TPU v7x, 32 devices: a whole 2x2x4 slice. The times are simulated.
32 devices in a mesh: clu: 32 (over z, y, x, core).
Axes of the slice: x: 2, y: 2, z: 4, core: 2. Of those that a mesh axis runs over, the one named last changes fastest.
Arguments:
- charges: bfloat16 [256, 32, 256], P('clu'), may hold values from -6 to 6
- basis: bfloat16 [256, 96, 256], P('clu'), may hold values from -0.375 to 0.375
- transfer: bfloat16 [256, 96, 96], P('clu'), may hold values from -0.4375 to 0.4375
- near_field: bfloat16 [256, 3, 256, 256], P('clu'), may hold values from -0.21875 to 0.21875
- coupling: bfloat16 [4096, 96, 96], P('clu'), may hold values from -0.625 to 0.625
- ranks: int32 [384], P('clu'), may hold values from 32 to 96, as said below
- block_source: int32 [4096], P('clu'), may hold values from 0 to 383, as said below
- block_target: int32 [4096], P('clu'), may hold values from 0 to 383, as said below
Outputs:
- first: bfloat16 [256, 32, 256], P('clu')
- second: bfloat16 [256, 32, 256], P('clu')
Inputs may be any that keep to these rules, and one draw needn't show every extreme that they name: `ranks`: each cluster's rank; 96 and 32 are both taken. `block_source`: global cluster numbers; a block's source and target are both leaves or both parents. Among the blocks of one device, at most 8 have their source on any one device, and exactly 8 for some device. `block_target`: global cluster numbers of the same level as the block's source. Among the blocks of one device, at most 8 have their target on any one device, and exactly 8 for some device.
All inputs are finite; a program needn't handle non-finite values.
Results may differ from a plain program's by a relative error of at most 0.025.
Values may be sent and summed in bfloat16 or wider, within the bound.
No kernel may reach another device: no remote copies, remote signals or barrier semaphores. Data moves between devices by JAX's collectives and lax.ppermute only.
A program may use at most 128 MiB of HBM per device.

v0:
```python
import jax
import jax.numpy as jnp
from jax import lax
from jax.sharding import PartitionSpec as P


def with_halo(cells, sides, width):
    for axis, dim in sides:
        count = lax.axis_size(axis)
        ends = count - 1
        head = lax.slice_in_dim(cells, 0, width, axis=dim)
        tail = lax.slice_in_dim(cells, cells.shape[dim] - width, cells.shape[dim], axis=dim)
        cells = jnp.concatenate(
            [
                lax.ppermute(tail, axis, [(i, (i + 1) % count) for i in range(ends)]),
                cells,
                lax.ppermute(head, axis, [((i + 1) % count, i) for i in range(ends)]),
            ],
            axis=dim,
        )
    return cells


def slot_ranking(devices):
    same = devices[:, None] == devices[None, :]
    positions = jnp.arange(devices.shape[0])
    earlier = positions[None, :] < positions[:, None]
    return jnp.sum((same & earlier).astype(jnp.int32), axis=1)


def local(charges, basis, transfer, near_field, coupling, ranks, block_source, block_target):
    leaves = basis.shape[0]
    rank_top = basis.shape[1]
    right_sides = charges.shape[1]
    clusters = ranks.shape[0]
    blocks = coupling.shape[0]
    devices_all = lax.axis_size("clu")
    per_peer = max(2, 2 * blocks // devices_all)
    slot_rows = per_peer * devices_all
    flat = right_sides * rank_top
    rank_mask = (jnp.arange(rank_top)[None, :] < ranks[:, None]).astype(jnp.float32)
    leaf_mask = rank_mask[:leaves][:, None, :]
    parent_mask = rank_mask[leaves:][:, None, :]
    target_dev = block_target // clusters
    back_rows = target_dev * per_peer + slot_ranking(target_dev)
    unused = jnp.full((slot_rows,), -1, jnp.int32)
    wanted_targets = unused.at[back_rows].set(block_target % clusters)
    owner_ids = lax.all_to_all(wanted_targets, "clu", split_axis=0, concat_axis=0, tiled=True)
    selector = (owner_ids[None, :] == jnp.arange(clusters)[:, None]).astype(jnp.float32)
    pairs = transfer.reshape(leaves // 2, 2, rank_top, rank_top)

    def pick_rows(piece):
        valid = (block_source >= 0) & (block_source < piece.shape[0])
        rows_now = piece[jnp.clip(block_source, 0, piece.shape[0] - 1)]
        return jnp.where(valid[:, None], rows_now, jnp.zeros_like(rows_now))

    def apply_matrix(field_in):
        leaf_coeff = jnp.einsum("irb,ikb->irk", field_in, basis, preferred_element_type=jnp.float32)
        leaf_coeff = (leaf_coeff * leaf_mask).astype(jnp.bfloat16)
        kids = leaf_coeff.reshape(leaves // 2, 2, right_sides, rank_top)
        parent_coeff = jnp.einsum("qcrk,qckp->qrp", kids, pairs, preferred_element_type=jnp.float32)
        parent_coeff = (parent_coeff * parent_mask).astype(jnp.bfloat16)
        coeffs = jnp.concatenate([leaf_coeff, parent_coeff], axis=0).reshape(clusters, flat)
        sources = pick_rows(lax.all_gather(coeffs, "clu", axis=0, tiled=True))
        terms = jnp.einsum(
            "jrk,jkp->jrp",
            sources.reshape(blocks, right_sides, rank_top),
            coupling,
            preferred_element_type=jnp.float32,
        ).reshape(blocks, flat)
        outbound = jnp.zeros((slot_rows, flat), jnp.float32).at[back_rows].set(terms)
        returned = lax.all_to_all(
            outbound.astype(jnp.bfloat16), "clu", split_axis=0, concat_axis=0, tiled=True
        ).astype(outbound.dtype)
        padded = with_halo(field_in, (("clu", 0),), 1)
        near_sum = jnp.einsum(
            "irb,iba->ira", padded[0:leaves], near_field[:, 0], preferred_element_type=jnp.float32
        )
        for offset in range(1, 3):
            near_sum = near_sum + jnp.einsum(
                "irb,iba->ira",
                padded[offset : offset + leaves],
                near_field[:, offset],
                preferred_element_type=jnp.float32,
            )
        summed = jnp.dot(
            selector, returned, precision=lax.Precision.HIGHEST, preferred_element_type=jnp.float32
        )
        field = (summed.reshape(clusters, right_sides, rank_top) * rank_mask[:, None, :]).astype(
            jnp.bfloat16
        )
        downward = jnp.einsum(
            "qrp,qckp->qcrk", field[leaves:], pairs, preferred_element_type=jnp.float32
        )
        leaf_total = field[:leaves].astype(jnp.float32) + downward.reshape(
            leaves, right_sides, rank_top
        )
        leaf_total = (leaf_total * leaf_mask).astype(jnp.bfloat16)
        far_sum = jnp.einsum("irk,ikb->irb", leaf_total, basis, preferred_element_type=jnp.float32)
        return (near_sum + far_sum).astype(jnp.bfloat16)

    first = apply_matrix(charges)
    second = apply_matrix(first)
    return (first, second)


def solution(mesh):
    in_specs = (
        P("clu", None, None),
        P("clu", None, None),
        P("clu", None, None),
        P("clu", None, None, None),
        P("clu", None, None),
        P("clu"),
        P("clu"),
        P("clu"),
    )
    out_specs = (P("clu", None, None), P("clu", None, None))
    return jax.shard_map(local, mesh=mesh, in_specs=in_specs, out_specs=out_specs, check_vma=False)
```

profile of v0, /device:TPU:0, one launch (start us, length us, event | category | flops | bytes accessed | tf_op | source)
XLA Modules:
  0.0 280.5 jit_solution(14040642673298452673)
XLA Ops:
  7.2 0.8 fusion.60
  8.0 0.2 copy-done
  8.2 1.1 fusion.10
  9.3 1.2 fusion.14
  10.5 0.8 reshape.132
  11.4 0.7 and_select_fusion
  12.0 0.2 convert_reduce_fusion
  12.2 1.0 scatter_custom_fusion
  13.2 0.7 all_to_all.22
  13.9 7.4 %all-to-all-start = ((s32[32,8,1]{1,2,0:T(1,128)}), s32[32,8,1]{1,2,0:T(1,128)}, u32[]{:S(2)}, u32[]{:S(2)}) async-start(s32[32,8,1]{1,2,0:T(1,128)} %bitcast.3), calls=%async_computation | async-start | bytes 32768 | tf_op jit(solution)/shard_map/all_to_all | solution.py:48
  21.4 4.7 %copy.58 = bf16[128,96,96]{2,1,0:T(8,128)(2,1)} copy(bf16[128,96,96]{0,2,1:T(8,128)(2,1)} %param.12) | data formatting | bytes 4718592 | tf_op args[4]
  26.1 0.6 compare_and_fusion
  26.7 46.4 %all-gather.5.cloned.1.call-done = bf16[32,12,3072]{2,1,0:T(8,128)(2,1)} async-done(((bf16[1,12,3072]{2,1,0:T(8,128)(2,1)}), bf16[32,12,3072]{2,1,0:T(8,128)(2,1)}) %all-gather.5.cloned.1.call-update) | async-done | bytes 2359312 | tf_op jit(solution)/shard_map/all_gather | solution.py:64
  73.2 2.8 %reshape.133 = bf16[384,3072]{1,0:T(8,128)(2,1)S(1)} reshape(bf16[32,12,3072]{2,1,0:T(8,128)(2,1)} %all-gather.5.cloned.1.call-done) | data formatting | bytes 4718592
  76.0 1.9 gather_fusion
  78.0 2.4 copy.56
  80.4 2.1 broadcast_select_fusion.1
  82.5 2.6 copy.57
  85.1 3.5 %fusion.69 = f32[128,32,96]{2,1,0:T(8,128)} fusion(bf16[128,32,96]{2,1,0:T(8,128)(2,1)} %copy.57, bf16[128,96,96]{2,1,0:T(8,128)(2,1)S(1)} %copy-done.1), kind=kOutput, calls=%fused_computation.100 | convolution fusion | flops 75497472 | bytes 4718592 | tf_op jit(solution)/shard_map/jrk,jkp->jrp/dot_general | solution.py:65
  88.6 2.1 copy.59
  90.7 1.6 copy.60
  92.3 3.1 %scatter_custom_fusion.1 = f32[256,3072]{1,0:T(8,128)S(1)} fusion(s32[128]{0:T(128)} %copy-done.15, f32[128,3072]{1,0:T(8,128)} %copy.60, f32[]{:T(128)} %constant.31.clone.1), kind=kCustom, calls=%fused_computation.9 | custom fusion | bytes 3146240 | tf_op jit(solution)/shard_map/scatter | solution.py:71
  95.5 1.4 convert_bitcast_fusion.1
  96.9 3.4 %all-to-all-start.1 = ((bf16[32,8,3072]{2,1,0:T(8,128)(2,1)}), bf16[32,8,3072]{2,1,0:T(8,128)(2,1)S(1)}, u32[]{:S(2)}, u32[]{:S(2)}) async-start(bf16[32,8,3072]{2,1,0:T(8,128)(2,1)} %convert_bitcast_fusion.1), calls=%async_computation.1 | async-start | bytes 3145728 | tf_op jit(solution)/shard_map/all_to_all | solution.py:72
  100.3 0.6 fusion.68
  101.0 1.3 collective-permute-start.1
  102.2 3.6 %collective-permute-start = (bf16[1,32,256]{2,1,0:T(8,128)(2,1)}, bf16[1,32,256]{2,1,0:T(8,128)(2,1)}, u32[]{:S(2)}, u32[]{:S(2)}) collective-permute-start(bf16[1,32,256]{2,1,0:T(8,128)(2,1)} %get-tuple-element.4), channel_id=1, source_target_pairs={{0,1},{1,2},{2,3},{3,4},{4,5},{5,6},{6,7},{7,8},{8,9},{9,10},{10,1... | collective-permute-start | bytes 49160 | tf_op jit(solution)/shard_map/ppermute | solution.py:15
  105.9 2.2 fusion.22
  108.1 0.5 broadcast.64
  108.6 1.4 reduce.3
  110.0 0.7 eq.33
  110.7 2.2 fusion.18
  112.9 25.1 %all-to-all-done.1 = bf16[32,8,3072]{2,1,0:T(8,128)(2,1)S(1)} async-done(((bf16[32,8,3072]{2,1,0:T(8,128)(2,1)}), bf16[32,8,3072]{2,1,0:T(8,128)(2,1)S(1)}, u32[]{:S(2)}, u32[]{:S(2)}) %all-to-all-start.1) | async-done | bytes 1572896 | tf_op jit(solution)/shard_map/all_to_all | solution.py:72
  138.0 0.7 copy.61
  138.7 1.3 fusion.56
  140.1 1.1 fusion.52
  141.3 0.2 fusion.70
  141.6 1.5 fusion.8
  143.1 0.2 fusion.11
  143.4 0.2 fusion.15
  143.8 0.8 reshape.134
  144.6 59.1 %all-gather.7.cloned.1.call-done = bf16[32,12,3072]{2,1,0:T(8,128)(2,1)} async-done(((bf16[1,12,3072]{2,1,0:T(8,128)(2,1)}), bf16[32,12,3072]{2,1,0:T(8,128)(2,1)}) %all-gather.7.cloned.1.call-update) | async-done | bytes 2359312 | tf_op jit(solution)/shard_map/all_gather | solution.py:64
  203.7 2.8 %reshape.135 = bf16[384,3072]{1,0:T(8,128)(2,1)S(1)} reshape(bf16[32,12,3072]{2,1,0:T(8,128)(2,1)} %all-gather.7.cloned.1.call-done) | data formatting | bytes 4718592
  206.6 2.0 gather_fusion.1
  208.6 2.4 copy.63
  211.1 2.1 broadcast_select_fusion
  213.1 2.6 copy.64
  215.7 3.5 %fusion.71 = f32[128,32,96]{2,1,0:T(8,128)} fusion(bf16[128,32,96]{2,1,0:T(8,128)(2,1)} %copy.64, bf16[128,96,96]{2,1,0:T(8,128)(2,1)S(1)} %copy-done.2), kind=kOutput, calls=%fused_computation.102 | convolution fusion | flops 75497472 | bytes 4718592 | tf_op jit(solution)/shard_map/jrk,jkp->jrp/dot_general | solution.py:65
  219.2 2.1 copy.66
  221.3 1.6 copy.67
  222.9 3.1 %scatter_custom_fusion.2 = f32[256,3072]{1,0:T(8,128)S(1)} fusion(s32[128]{0:T(128)} %copy-done.15, f32[128,3072]{1,0:T(8,128)} %copy.67, f32[]{:T(128)} %constant.31.clone.1), kind=kCustom, calls=%fused_computation.7 | custom fusion | bytes 3146240 | tf_op jit(solution)/shard_map/scatter | solution.py:71
  226.1 1.4 convert_bitcast_fusion
  227.5 3.4 %all-to-all-start.2 = ((bf16[32,8,3072]{2,1,0:T(8,128)(2,1)}), bf16[32,8,3072]{2,1,0:T(8,128)(2,1)S(1)}, u32[]{:S(2)}, u32[]{:S(2)}) async-start(bf16[32,8,3072]{2,1,0:T(8,128)(2,1)} %convert_bitcast_fusion), calls=%async_computation.2 | async-start | bytes 3145728 | tf_op jit(solution)/shard_map/all_to_all | solution.py:72
  230.9 0.6 fusion.67
  231.5 1.4 collective-permute-start.3
  232.9 2.2 fusion.20
  235.2 3.6 %collective-permute-start.2 = (bf16[1,32,256]{2,1,0:T(8,128)(2,1)}, bf16[1,32,256]{2,1,0:T(8,128)(2,1)}, u32[]{:S(2)}, u32[]{:S(2)}) collective-permute-start(bf16[1,32,256]{2,1,0:T(8,128)(2,1)} %get-tuple-element.2), channel_id=1, source_target_pairs={{0,1},{1,2},{2,3},{3,4},{4,5},{5,6},{6,7},{7,8},{8,9},{9,10},{10,1... | collective-permute-start | bytes 49160 | tf_op jit(solution)/shard_map/ppermute | solution.py:15
  238.8 2.2 fusion.16
  241.0 27.6 %all-to-all-done.2 = bf16[32,8,3072]{2,1,0:T(8,128)(2,1)S(1)} async-done(((bf16[32,8,3072]{2,1,0:T(8,128)(2,1)}), bf16[32,8,3072]{2,1,0:T(8,128)(2,1)S(1)}, u32[]{:S(2)}, u32[]{:S(2)}) %all-to-all-start.2) | async-done | bytes 1572896 | tf_op jit(solution)/shard_map/all_to_all | solution.py:72
  268.6 0.7 copy.68
  269.4 0.6 fusion.54
  270.0 1.1 fusion.51
  271.2 0.2 fusion.72
  271.5 2.2 fusion.9
  (55 shorter events, 0.7 us)
Async XLA Ops:
  7.2 1.0 copy-start
  7.2 66.0 %all-gather.5.cloned.1.call-start = ((), (), s32[]{:S(2)}) async-start(), calls=%async_computation.3 | async-start | bytes 3244032 | tf_op jit(solution)/shard_map/all_gather | solution.py:64
  9.3 16.8 %copy-start.14 = (s32[128]{0:T(128)S(1)}, s32[128]{0:T(128)}, u32[]{:S(2)}) copy-start(s32[128]{0:T(128)} %param.14) | copy-start | bytes 1540
  12.2 63.8 %copy-start.15 = (s32[128]{0:T(128)}, s32[128]{0:T(128)S(1)}, u32[]{:S(2)}) copy-start(s32[128]{0:T(128)S(1)} %compare_select_fusion.1) | copy-start | bytes 1540
  13.9 82.9 %all-to-all-start = ((s32[32,8,1]{1,2,0:T(1,128)}), s32[32,8,1]{1,2,0:T(1,128)}, u32[]{:S(2)}, u32[]{:S(2)}) async-start(s32[32,8,1]{1,2,0:T(1,128)} %bitcast.3), calls=%async_computation | async-start | bytes 32768 | tf_op jit(solution)/shard_map/all_to_all | solution.py:48
  26.1 49.9 %copy-start.12 = (s32[1024]{0:T(1024)}, s32[1024]{0:T(1024)S(1)}, u32[]{:S(2)}) copy-start(s32[1024]{0:T(1024)S(1)} %pad_clamp_fusion) | copy-start | bytes 12292
  78.0 7.2 %copy-start.1 = (bf16[128,96,96]{2,1,0:T(8,128)(2,1)S(1)}, bf16[128,96,96]{2,1,0:T(8,128)(2,1)}, u32[]{:S(2)}) copy-start(bf16[128,96,96]{2,1,0:T(8,128)(2,1)} %copy.58) | copy-start | bytes 7077892
  96.9 3.5 %copy-start.4 = (bf16[8,32,256]{2,1,0:T(8,128)(2,1)S(1)}, bf16[8,32,256]{2,1,0:T(8,128)(2,1)}, u32[]{:S(2)}) copy-start(bf16[8,32,256]{2,1,0:T(8,128)(2,1)} %param.8) | copy-start | bytes 393220
  96.9 41.1 %all-to-all-start.1 = ((bf16[32,8,3072]{2,1,0:T(8,128)(2,1)}), bf16[32,8,3072]{2,1,0:T(8,128)(2,1)S(1)}, u32[]{:S(2)}, u32[]{:S(2)}) async-start(bf16[32,8,3072]{2,1,0:T(8,128)(2,1)} %convert_bitcast_fusion.1), calls=%async_computation.1 | async-start | bytes 3145728 | tf_op jit(solution)/shard_map/all_to_all | solution.py:72
  100.3 103.4 %all-gather.7.cloned.1.call-start = ((), (), s32[]{:S(2)}) async-start(), calls=%async_computation.4 | async-start | bytes 3244032 | tf_op jit(solution)/shard_map/all_gather | solution.py:64
  101.0 9.7 %collective-permute-start.1 = (bf16[1,32,256]{2,1,0:T(8,128)(2,1)S(1)}, bf16[1,32,256]{2,1,0:T(8,128)(2,1)S(1)}, u32[]{:S(2)}, u32[]{:S(2)}) collective-permute-start(bf16[1,32,256]{2,1,0:T(8,128)(2,1)S(1)} %get-tuple-element.5), channel_id=1, source_target_pairs={{1,0},{2,1},{3,2},{4,3},{5,4},{6,5},{7,6},{8,7},{9,8},{10,9},{11,1... | collective-permute-start | bytes 49160 | tf_op jit(solution)/shard_map/ppermute | solution.py:17
  102.2 39.3 %collective-permute-start = (bf16[1,32,256]{2,1,0:T(8,128)(2,1)}, bf16[1,32,256]{2,1,0:T(8,128)(2,1)}, u32[]{:S(2)}, u32[]{:S(2)}) collective-permute-start(bf16[1,32,256]{2,1,0:T(8,128)(2,1)} %get-tuple-element.4), channel_id=1, source_target_pairs={{0,1},{1,2},{2,3},{3,4},{4,5},{5,6},{6,7},{7,8},{8,9},{9,10},{10,1... | collective-permute-start | bytes 49160 | tf_op jit(solution)/shard_map/ppermute | solution.py:15
  138.7 2.9 %copy-start.5 = (bf16[8,32,256]{2,1,0:T(8,128)(2,1)S(1)}, bf16[8,32,256]{2,1,0:T(8,128)(2,1)}, u32[]{:S(2)}) copy-start(bf16[8,32,256]{2,1,0:T(8,128)(2,1)} %param.8) | copy-start | bytes 393220
  138.7 2.9 %copy-start.9 = (f32[8,32,256]{2,1,0:T(8,128)S(1)}, f32[8,32,256]{2,1,0:T(8,128)}, u32[]{:S(2)}) copy-start(f32[8,32,256]{2,1,0:T(8,128)} %fusion.22) | copy-start | bytes 786436
  138.7 2.9 %copy-start.17 = (f32[8,32,256]{2,1,0:T(8,128)S(1)}, f32[8,32,256]{2,1,0:T(8,128)}, u32[]{:S(2)}) copy-start(f32[8,32,256]{2,1,0:T(8,128)} %fusion.18) | copy-start | bytes 786436
  138.7 4.6 %copy-start.3 = (bf16[8,96,96]{2,1,0:T(8,128)(2,1)S(1)}, bf16[8,96,96]{2,1,0:T(8,128)(2,1)}, u32[]{:S(2)}) copy-start(bf16[8,96,96]{2,1,0:T(8,128)(2,1)} %param.10) | copy-start | bytes 442372
  143.1 0.7 copy-start.6
  206.5 4.5 %copy-start.13 = (pred[128]{0:T(512)(128)(4,1)S(1)}, pred[128]{0:T(512)(128)(4,1)}, u32[]{:S(2)}) copy-start(pred[128]{0:T(512)(128)(4,1)} %compare_and_fusion) | copy-start | bytes 388
  208.6 7.1 %copy-start.2 = (bf16[128,96,96]{2,1,0:T(8,128)(2,1)S(1)}, bf16[128,96,96]{2,1,0:T(8,128)(2,1)}, u32[]{:S(2)}) copy-start(bf16[128,96,96]{2,1,0:T(8,128)(2,1)} %copy.58) | copy-start | bytes 7077892
  227.5 3.4 %copy-start.7 = (bf16[8,32,256]{2,1,0:T(8,128)(2,1)S(1)}, bf16[8,32,256]{2,1,0:T(8,128)(2,1)}, u32[]{:S(2)}) copy-start(bf16[8,32,256]{2,1,0:T(8,128)(2,1)} %copy-done.6) | copy-start | bytes 393220
  227.5 41.2 %all-to-all-start.2 = ((bf16[32,8,3072]{2,1,0:T(8,128)(2,1)}), bf16[32,8,3072]{2,1,0:T(8,128)(2,1)S(1)}, u32[]{:S(2)}, u32[]{:S(2)}) async-start(bf16[32,8,3072]{2,1,0:T(8,128)(2,1)} %convert_bitcast_fusion), calls=%async_computation.2 | async-start | bytes 3145728 | tf_op jit(solution)/shard_map/all_to_all | solution.py:72
  231.5 37.8 %copy-start.11 = (s32[256]{0:T(256)S(1)}, s32[256]{0:T(256)}, u32[]{:S(2)}) copy-start(s32[256]{0:T(256)} %eq.33) | copy-start | bytes 3076
  231.5 7.3 %collective-permute-start.3 = (bf16[1,32,256]{2,1,0:T(8,128)(2,1)S(1)}, bf16[1,32,256]{2,1,0:T(8,128)(2,1)S(1)}, u32[]{:S(2)}, u32[]{:S(2)}) collective-permute-start(bf16[1,32,256]{2,1,0:T(8,128)(2,1)S(1)} %get-tuple-element.3), channel_id=1, source_target_pairs={{1,0},{2,1},{3,2},{4,3},{5,4},{6,5},{7,6},{8,7},{9,8},{10,9},{11,1... | collective-permute-start | bytes 49160 | tf_op jit(solution)/shard_map/ppermute | solution.py:17
  235.2 36.3 %collective-permute-start.2 = (bf16[1,32,256]{2,1,0:T(8,128)(2,1)}, bf16[1,32,256]{2,1,0:T(8,128)(2,1)}, u32[]{:S(2)}, u32[]{:S(2)}) collective-permute-start(bf16[1,32,256]{2,1,0:T(8,128)(2,1)} %get-tuple-element.2), channel_id=1, source_target_pairs={{0,1},{1,2},{2,3},{3,4},{4,5},{5,6},{6,7},{7,8},{8,9},{9,10},{10,1... | collective-permute-start | bytes 49160 | tf_op jit(solution)/shard_map/ppermute | solution.py:15
  269.3 2.1 copy-start.8
  269.3 2.1 copy-start.10
  269.3 2.1 copy-start.16
Sparse Core Ops, SparseCore 0:
  11.5 61.6 all-gather.4
  144.7 58.9 all-gather.6
where the time goes:
time: 282 us; the launch traced here: 280 us
  waiting for transfers between devices  158 us (56%)
  local copies, waits for them, and re-layouts  45.7 us (16%)
  matrix products  26.9 us (10%)
  starting transfers between devices  24.3 us (9%)
  between operations  14.5 us (5%)
  other arithmetic  10.8 us (4%)
    all_gather x2, waiting for transfers between devices, apply_matrix(): sources = pick_rows(lax.all_gather(coeffs, 'clu', axis=0, tiled=True))  106 us
    all_to_all x2, waiting for transfers between devices, apply_matrix(): lax.all_to_all(outbound.astype(jnp.bfloat16), 'clu', split_axis=0, concat...  52.8 us
    unnamed x41, local copies, waits for them, and re-layouts  12.5 us
    gather x4, local copies, waits for them, and re-layouts, pick_rows(): rows_now = piece[jnp.clip(block_source, 0, piece.shape[0] - 1)]  8.86 us
    dot_general x4, matrix products, apply_matrix(): jnp.einsum('irb,iba->ira', padded[offset:offset + leaves], near_field[:,...  8.84 us
    all_to_all x1, starting transfers between devices, local(): lax.all_to_all(wanted_targets, 'clu', split_axis=0, concat_axis=0, tiled=...  7.43 us
    ppermute x2, starting transfers between devices, with_halo(): lax.ppermute(tail, axis, [(i, (i + 1) % count) for i in range(ends)])  7.25 us
    dot_general x2, matrix products, apply_matrix(): jnp.einsum('jrk,jkp->jrp', sources.reshape(blocks, right_sides, rank_top)...  7.04 us
  transfers between devices with their start and end apart: 9, of which 4 were waited for; matrix products, arithmetic and copies ran while one was open for 18% of the time, Pallas kernels for 0%

commit v1 on v0

v1 whole, which is shorter than its diff:
```python
import functools

import jax
import jax.numpy as jnp
from jax import lax
from jax.experimental import pallas as pl
from jax.experimental.pallas import tpu as pltpu
from jax.sharding import PartitionSpec as P

LANES = 128
BF = jnp.bfloat16
F32 = jnp.float32
VMEM = pl.BlockSpec(memory_space=pltpu.VMEM)
SMEM = pl.BlockSpec(memory_space=pltpu.SMEM)


def dot(a, b):
    return lax.dot_general(a, b, (((1,), (0,)), ((), ())), preferred_element_type=F32)


def dot_t(a, b):
    return lax.dot_general(a, b, (((1,), (1,)), ((), ())), preferred_element_type=F32)


def spread(rank_top, piece):
    third = LANES - rank_top
    row = lax.broadcasted_iota(jnp.int32, (rank_top, LANES), 0)
    lane = lax.broadcasted_iota(jnp.int32, (rank_top, LANES), 1)
    hit = (lane - rank_top == row - third * piece) & (lane >= rank_top)
    return hit.astype(F32).astype(BF)


def collect(rank_top, piece):
    third = LANES - rank_top
    row = lax.broadcasted_iota(jnp.int32, (LANES, LANES), 0)
    lane = lax.broadcasted_iota(jnp.int32, (LANES, LANES), 1)
    hit = (row - rank_top == lane - third * piece) & (row >= rank_top)
    return hit.astype(F32).astype(BF)


def emit_coeffs(read_leaf, basis_ref, transfer_ref, ranks_ref, out_ref, leaves, rank_top):
    rhs = out_ref.shape[1]
    lane = lax.broadcasted_iota(jnp.int32, (rhs, rank_top), 1)
    coeffs = []
    for i in range(leaves):
        value = dot_t(read_leaf(i), basis_ref[i])
        coeffs.append(jnp.where(lane < ranks_ref[i], value, 0.0).astype(BF))
    for q in range(leaves // 2):
        value = dot(coeffs[2 * q], transfer_ref[2 * q]) + dot(coeffs[2 * q + 1], transfer_ref[2 * q + 1])
        coeffs.append(jnp.where(lane < ranks_ref[leaves + q], value, 0.0).astype(BF))
    mains = out_ref.shape[0]
    for q in range(mains // 3):
        for k in range(3):
            tile = dot(coeffs[mains + q], spread(rank_top, k)).astype(BF)
            out_ref[3 * q + k] = tile
            out_ref[3 * q + k, :, :rank_top] = coeffs[3 * q + k]


def coeff_kernel(ranks_ref, v_ref, basis_ref, transfer_ref, out_ref):
    leaves, rank_top, _ = basis_ref.shape
    emit_coeffs(lambda i: v_ref[i], basis_ref, transfer_ref, ranks_ref, out_ref, leaves, rank_top)


def slots_kernel(targets_ref, ids_ref, slots_ref, counts, *, clusters, per_peer):
    blocks = targets_ref.shape[0]
    peers = ids_ref.shape[0] // per_peer

    def reset(i, _):
        counts[i] = 0
        return 0

    def unused(i, _):
        ids_ref[i] = clusters
        return 0

    def place(j, _):
        target = targets_ref[j]
        peer = lax.div(target, jnp.int32(clusters))
        slot = peer * per_peer + counts[peer]
        counts[peer] = counts[peer] + 1
        ids_ref[slot] = target - peer * clusters
        slots_ref[j] = slot
        return 0

    lax.fori_loop(0, peers, reset, 0)
    lax.fori_loop(0, peers * per_peer, unused, 0)
    lax.fori_loop(0, blocks, place, 0)


def unpack(packed_ref, pads_ref, rank_top, step):
    groups, rhs, _ = pads_ref.shape
    pieces = [collect(rank_top, k) for k in range(3)]

    def some(s, _):
        total = None
        for k in range(3):
            tiles = jnp.concatenate([packed_ref[(s * step + g) * 3 + k] for g in range(step)], axis=0)
            part = dot(tiles, pieces[k])
            total = part if total is None else total + part
        total = total.astype(BF).reshape(step, rhs, LANES)
        for g in range(step):
            pads_ref[s * step + g] = total[g]
        return 0

    lax.fori_loop(0, groups // step, some, 0)


def couple_kernel(main_ref, pad_ref, is_pad_ref, slot_ref, gathered_ref, coupling_ref, out_ref, pads, terms, *, unroll):
    blocks, rank_top, _ = coupling_ref.shape
    rhs = out_ref.shape[1]
    slots = terms.shape[0]
    unpack(gathered_ref, pads, rank_top, 8)

    def clear(s, _):
        for u in range(8):
            terms[s * 8 + u] = jnp.zeros((rhs, LANES), BF)
        return 0

    lax.fori_loop(0, slots // 8, clear, 0)

    def some(s, _):
        for u in range(unroll):
            j = s * unroll + u
            main = gathered_ref[main_ref[j], :, :rank_top]
            pad = pads[pad_ref[j], :, :rank_top]
            source = jnp.where(is_pad_ref[j] > 0, pad, main)
            terms[slot_ref[j], :, :rank_top] = dot(source, coupling_ref[j]).astype(BF)
        return 0

    lax.fori_loop(0, blocks // unroll, some, 0)

    pieces = [spread(rank_top, k) for k in range(3)]
    step = 8
    low = lax.broadcasted_iota(jnp.int32, (rhs, LANES), 1) < rank_top

    def pack(s, _):
        fourth = jnp.concatenate([terms[(s * step + g) * 4 + 3, :, :rank_top] for g in range(step)], axis=0)
        for k in range(3):
            moved = dot(fourth, pieces[k]).astype(BF).reshape(step, rhs, LANES)
            for g in range(step):
                quad = s * step + g
                out_ref[quad * 3 + k] = jnp.where(low, terms[quad * 4 + k], moved[g])
        return 0

    lax.fori_loop(0, slots // 4 // step, pack, 0)


def near_kernel(v_ref, before_ref, after_ref, near_ref, out_ref):
    leaves = v_ref.shape[0]
    for i in range(leaves):
        left = v_ref[i - 1] if i > 0 else before_ref[0]
        right = v_ref[i + 1] if i < leaves - 1 else after_ref[0]
        out_ref[i] = dot(left, near_ref[i, 0]) + dot(v_ref[i], near_ref[i, 1]) + dot(right, near_ref[i, 2])


def field_kernel(ids_ref, ranks_ref, terms_ref, near_ref, basis_ref, transfer_ref, out_ref, *rest):
    *coeff_ref, pads, total = rest
    leaves, rank_top, _ = basis_ref.shape
    rhs = out_ref.shape[1]
    clusters = leaves + leaves // 2
    unpack(terms_ref, pads, rank_top, 8)
    for c in range(clusters + 1):
        total[c] = jnp.zeros((rhs, LANES), F32)

    def add(quad, _):
        for k in range(3):
            at = ids_ref[quad * 4 + k]
            total[at] = total[at] + terms_ref[quad * 3 + k].astype(F32)
        at = ids_ref[quad * 4 + 3]
        total[at] = total[at] + pads[quad].astype(F32)
        return 0

    lax.fori_loop(0, pads.shape[0], add, 0, unroll=4)

    lane = lax.broadcasted_iota(jnp.int32, (rhs, rank_top), 1)
    fields = [
        jnp.where(lane < ranks_ref[c], total[c, :, :rank_top], 0.0).astype(BF) for c in range(clusters)
    ]
    for i in range(leaves):
        down = fields[i].astype(F32) + dot_t(fields[leaves + i // 2], transfer_ref[i])
        leaf_total = jnp.where(lane < ranks_ref[i], down, 0.0).astype(BF)
        out_ref[i] = (near_ref[i] + dot(leaf_total, basis_ref[i])).astype(BF)
    if coeff_ref:
        emit_coeffs(
            lambda i: out_ref[i], basis_ref, transfer_ref, ranks_ref, coeff_ref[0], leaves, rank_top
        )


def params(mebibytes):
    return pltpu.CompilerParams(vmem_limit_bytes=mebibytes << 20)


def local(charges, basis, transfer, near_field, coupling, ranks, block_source, block_target):
    leaves, rank_top, width = basis.shape
    rhs = charges.shape[1]
    clusters = ranks.shape[0]
    blocks = coupling.shape[0]
    devices = lax.axis_size("clu")
    mains = clusters * 3 // 4
    per_peer = max(2, 2 * blocks // devices)
    per_peer = (per_peer + 3) // 4 * 4
    slots = per_peer * devices
    shape = jax.ShapeDtypeStruct

    cores, chips = 2, 4
    planes = devices // (cores * chips)
    plane_groups = [[p * cores * chips + r for p in range(planes)] for r in range(cores * chips)]
    chip_groups = [
        [p * cores * chips + c * cores + k for c in range(chips)] for p in range(planes) for k in range(cores)
    ]
    core_groups = [[h * cores + k for k in range(cores)] for h in range(devices // cores)]

    def gather(coeffs):
        for groups in (plane_groups, chip_groups, core_groups):
            coeffs = lax.all_gather(coeffs, "clu", axis=0, tiled=True, axis_index_groups=groups)
        return coeffs

    source_dev = block_source // clusters
    source_loc = block_source % clusters
    place = ((source_dev % cores) * chips + (source_dev // cores) % chips) * planes + source_dev // (cores * chips)
    is_pad = (source_loc >= mains).astype(jnp.int32)
    main_row = place * mains + jnp.where(source_loc >= mains, 0, source_loc)
    pad_row = place * (clusters - mains) + jnp.where(source_loc >= mains, source_loc - mains, 0)

    coeff_shape = shape((mains, rhs, LANES), BF)
    out_shape = shape((leaves, rhs, width), BF)
    first_coeffs = pl.pallas_call(
        coeff_kernel,
        out_shape=coeff_shape,
        in_specs=[SMEM, VMEM, VMEM, VMEM],
        out_specs=VMEM,
        compiler_params=params(16),
    )(ranks, charges, basis, transfer)

    wanted, slot_rows = pl.pallas_call(
        functools.partial(slots_kernel, clusters=clusters, per_peer=per_peer),
        out_shape=[shape((slots,), jnp.int32), shape((blocks,), jnp.int32)],
        in_specs=[SMEM],
        out_specs=[SMEM, SMEM],
        scratch_shapes=[pltpu.SMEM((devices,), jnp.int32)],
    )(block_target)
    owner_ids = lax.all_to_all(
        wanted.reshape(devices, per_peer), "clu", split_axis=0, concat_axis=0, tiled=True
    ).reshape(slots)

    couple = pl.pallas_call(
        functools.partial(couple_kernel, unroll=8),
        out_shape=shape((slots // 4 * 3, rhs, LANES), BF),
        in_specs=[SMEM, SMEM, SMEM, SMEM, VMEM, VMEM],
        out_specs=VMEM,
        scratch_shapes=[
            pltpu.VMEM((devices * (clusters - mains), rhs, LANES), BF),
            pltpu.VMEM((slots, rhs, LANES), BF),
        ],
        compiler_params=params(32),
        cost_estimate=pl.CostEstimate(
            flops=2 * blocks * rhs * rank_top * rank_top, bytes_accessed=10 << 20, transcendentals=0
        ),
    )

    near = pl.pallas_call(
        near_kernel,
        out_shape=shape((leaves, rhs, width), F32),
        in_specs=[VMEM] * 4,
        out_specs=VMEM,
        compiler_params=params(16),
        cost_estimate=pl.CostEstimate(
            flops=2 * leaves * 3 * rhs * width * width, bytes_accessed=4 << 20, transcendentals=0
        ),
    )

    def finish(with_coeffs):
        return pl.pallas_call(
            field_kernel,
            out_shape=[out_shape, coeff_shape] if with_coeffs else [out_shape],
            in_specs=[SMEM, SMEM, VMEM, VMEM, VMEM, VMEM],
            out_specs=[VMEM, VMEM] if with_coeffs else [VMEM],
            scratch_shapes=[
                pltpu.VMEM((slots // 4, rhs, LANES), BF),
                pltpu.VMEM((clusters + 1, rhs, LANES), F32),
            ],
            compiler_params=params(24),
        )

    ends = devices - 1

    def apply_matrix(field_in, coeffs, with_coeffs):
        gathered = gather(coeffs)
        outbound = couple(main_row, pad_row, is_pad, slot_rows, gathered, coupling)
        returned = lax.all_to_all(
            outbound.reshape(devices, per_peer * 3 // 4, rhs, LANES), "clu", split_axis=0, concat_axis=0, tiled=True
        ).reshape(slots // 4 * 3, rhs, LANES)
        before = lax.ppermute(field_in[leaves - 1 :], "clu", [(i, i + 1) for i in range(ends)])
        after = lax.ppermute(field_in[:1], "clu", [(i + 1, i) for i in range(ends)])
        near_sum = near(field_in, before, after, near_field)
        return finish(with_coeffs)(owner_ids, ranks, returned, near_sum, basis, transfer)

    first, second_coeffs = apply_matrix(charges, first_coeffs, True)
    (second,) = apply_matrix(first, second_coeffs, False)
    return (first, second)


def solution(mesh):
    in_specs = (
        P("clu", None, None),
        P("clu", None, None),
        P("clu", None, None),
        P("clu", None, None, None),
        P("clu", None, None),
        P("clu"),
        P("clu"),
        P("clu"),
    )
    out_specs = (P("clu", None, None), P("clu", None, None))
    return jax.shard_map(local, mesh=mesh, in_specs=in_specs, out_specs=out_specs, check_vma=False)
```

time: 282 us -> 263 us (0.933)
  blocking collectives: 0 us -> 36.7 us
  Pallas kernels: 0 us -> 34.3 us
  waiting for transfers between devices: 158 us -> 124 us
  matrix products: 26.9 us -> 0 us
  local copies, waits for them, and re-layouts: 45.7 us -> 28.2 us
  other arithmetic: 10.8 us -> 0.74 us
    all_gather x2 -> x4, waiting for transfers between devices: 106 us -> 66.2 us  [gather(): lax.all_gather(coeffs, 'clu', axis=0, tiled=True, axis_index_groups=groups)]
    all_gather x0 -> x2, blocking collectives: none -> 36.7 us  [gather(): lax.all_gather(coeffs, 'clu', axis=0, tiled=True, axis_index_groups=groups)]
    pallas_call x0 -> x8, Pallas kernels: none -> 34.3 us  [the longest x2 15 us: apply_matrix(): outbound = couple(main_row, pad_row, is_pad, slot_rows, gathered, coupling)]
    dot_general x18 -> x0, matrix products: 26.9 us -> none  [the longest x4 8.84 us: apply_matrix(): jnp.einsum('irb,iba->ira', padded[offset:offset + leaves], near_field[:,...]
    unnamed x41 -> x69, local copies, waits for them, and re-layouts: 12.5 us -> 24.1 us
    gather x4 -> x0, local copies, waits for them, and re-layouts: 8.86 us -> none  [pick_rows(): rows_now = piece[jnp.clip(block_source, 0, piece.shape[0] - 1)]]
    scatter x3 -> x0, local copies, waits for them, and re-layouts: 7.21 us -> none  [the longest x2 6.23 us: apply_matrix(): jnp.zeros((slot_rows, flat), jnp.float32).at[back_rows].set(terms)]
    dot_general x4 -> x0, local copies, waits for them, and re-layouts: 5.48 us -> none  [the longest x2 4.11 us: apply_matrix(): jnp.einsum('jrk,jkp->jrp', sources.reshape(blocks, right_sides, rank_top)...]
  transfers between devices with their start and end apart: 9 -> 11, of which waited for: 4 -> 7; matrix products, arithmetic and copies ran while one was open for 18% -> 3% of each run, Pallas kernels for 0% -> 5%
where the time goes in v1:
time: 263 us; the launch traced here: 261 us
  waiting for transfers between devices  124 us (47%)
  blocking collectives  36.7 us (14%)
  Pallas kernels  34.3 us (13%)
  local copies, waits for them, and re-layouts  28.2 us (11%)
  starting transfers between devices  23.3 us (9%)
  between operations  14.1 us (5%)
    all_gather x4, waiting for transfers between devices, gather(): lax.all_gather(coeffs, 'clu', axis=0, tiled=True, axis_index_groups=groups)  66.2 us
    all_to_all x2, waiting for transfers between devices, apply_matrix(): lax.all_to_all(outbound.reshape(devices, per_peer * 3 // 4, rhs, LANES),...  53.6 us
    all_gather x2, blocking collectives, gather(): lax.all_gather(coeffs, 'clu', axis=0, tiled=True, axis_index_groups=groups)  36.7 us
    unnamed x69, local copies, waits for them, and re-layouts  24.1 us
    pallas_call x2, Pallas kernels, apply_matrix(): outbound = couple(main_row, pad_row, is_pad, slot_rows, gathered, coupling)  15 us
    pallas_call x2, Pallas kernels, apply_matrix(): finish(with_coeffs)(owner_ids, ranks, returned, near_sum, basis, transfer)  12.4 us
    all_to_all x2, starting transfers between devices, apply_matrix(): lax.all_to_all(outbound.reshape(devices, per_peer * 3 // 4, rhs, LANES),...  11.8 us
  transfers between devices with their start and end apart: 11, of which 7 were waited for; matrix products, arithmetic and copies ran while one was open for 3% of the time, Pallas kernels for 5%

profile of v1, /device:TPU:0, one launch (start us, length us, event | category | flops | bytes accessed | tf_op | source)
XLA Modules:
  0.0 261.1 jit_solution(6564826056935516297)
XLA Ops:
  7.2 0.0 all-gather.5.cloned.1.call-start
  7.2 0.0 copy-start.4
  7.2 1.0 copy-done.4
  8.2 0.9 copy-done.8
  9.1 0.9 copy-done.15
  10.0 0.7 copy-done.24
  10.7 1.0 shard_map.96
  11.7 16.3 %all_gather.18 = bf16[36,32,128]{2,1,0:T(8,128)(2,1)} all-gather(bf16[9,32,128]{2,1,0:T(8,128)(2,1)S(1)} %shard_map.96), channel_id=1, replica_groups={{0,8,16,24},{1,9,17,25},{2,10,18,26},{3,11,19,27},{4,12,20,28},{5,13,21..., dimensions={0}, use_global_device_ids=true | all-gather | bytes 368640 | tf_op jit(solution)/shard_map/all_gather | solution.py:215
  28.1 0.0 all-gather.5.cloned.1.call-update
  28.1 0.0 all-gather.7.cloned.1.call-start
  28.1 29.6 %all-gather.5.cloned.1.call-done = bf16[144,32,128]{2,1,0:T(8,128)(2,1)} async-done(((bf16[36,32,128]{2,1,0:T(8,128)(2,1)}), bf16[144,32,128]{2,1,0:T(8,128)(2,1)}) %all-gather.5.cloned.1.call-update) | async-done | bytes 1179664 | tf_op jit(solution)/shard_map/all_gather | solution.py:215
  57.7 0.0 all-gather.7.cloned.1.call-update
  57.7 4.6 %shard_map.95 = (s32[256]{0:T(256)}, s32[128]{0:T(128)}) custom-call(s32[128]{0:T(128)} %targets_ref.1), custom_call_target="tpu_custom_call" | custom-call | tf_op jit(solution)/shard_map/pallas_call | solution.py:235
  62.3 1.4 all_to_all.12
  63.7 4.6 %all-to-all-start = ((s32[32,1,8]{2,1,0:T(1,128)}), s32[32,1,8]{2,1,0:T(1,128)S(1)}, u32[]{:S(2)}, u32[]{:S(2)}) async-start(s32[32,1,8]{2,1,0:T(1,128)} %bitcast), calls=%async_computation | async-start | bytes 32768 | tf_op jit(solution)/shard_map/all_to_all | solution.py:242
  68.3 0.0 copy-start.33
  68.3 3.5 %copy.15.coupling_ref = bf16[128,96,96]{2,1,0:T(8,128)(2,1)S(1)} copy(bf16[128,96,96]{0,2,1:T(8,128)(2,1)} %param.12) | data formatting | bytes 4718592 | tf_op args[4]
  72.0 0.0 all-gather.7.cloned.1.call-done.gathered_ref
  72.0 1.7 copy-done.6
  73.7 7.5 %shard_map.97 = bf16[192,32,128]{2,1,0:T(8,128)(2,1)S(1)} custom-call(s32[128]{0:T(128)S(1)} %fusion.1.main_ref, s32[128]{0:T(128)S(1)} %get-tuple-element.12.pad_ref, s32[128]{0:T(128)S(1)} %get-tuple-element.10.is_pad_ref, s32[128]{0:T(128)S(1)} %copy-done.27, bf16[288,32,128]{2,1,0:T(8,128)(2,1)S(1)} %copy-done.6, bf16[128,96,96]{2,1,0:T(8,128)(2,1)S(1)} %copy.15.coupling_ref), custom_call_target="tpu_custom_call" | custom-call | flops 75497472 | bytes 10485760 | tf_op jit(solution)/shard_map/pallas_call | solution.py:289
  81.2 1.1 copy-done.2
  82.4 6.0 %all-to-all-start.1 = ((bf16[32,6,32,128]{3,2,1,0:T(8,128)(2,1)}), bf16[32,6,32,128]{3,2,1,0:T(8,128)(2,1)}, u32[]{:S(2)}, u32[]{:S(2)}) async-start(bf16[32,6,32,128]{3,2,1,0:T(8,128)(2,1)} %bitcast.5), calls=%async_computation.1 | async-start | bytes 3145728 | tf_op jit(solution)/shard_map/all_to_all | solution.py:290
  88.3 0.0 all-gather.9.cloned.1.call-start
  88.4 0.7 fusion.6
  89.1 2.1 collective-permute-start
  91.2 1.3 collective-permute-start.1
  92.5 0.5 broadcast.39
  93.0 0.7 reduce.3
  93.7 0.7 reshape.24.ids_ref
  94.4 1.0 collective-permute-done.1.after_ref
  95.4 0.6 copy-done.18
  96.0 1.9 copy-done
  97.9 0.9 copy-done.16
  98.8 0.7 copy-done.19
  99.5 0.6 shard_map.98.near_ref
  100.2 0.7 copy-done.11
  100.9 25.2 %all-to-all-done.1 = bf16[32,6,32,128]{3,2,1,0:T(8,128)(2,1)} async-done(((bf16[32,6,32,128]{3,2,1,0:T(8,128)(2,1)}), bf16[32,6,32,128]{3,2,1,0:T(8,128)(2,1)}, u32[]{:S(2)}, u32[]{:S(2)}) %all-to-all-start.1) | async-done | bytes 1572896 | tf_op jit(solution)/shard_map/all_to_all | solution.py:290
  126.1 0.9 copy-done.9
  127.0 0.9 copy-done.12
  127.9 0.7 copy-done.20
  128.6 0.7 copy-done.25
  129.3 6.2 %shard_map.99 = (bf16[8,32,256]{2,1,0:T(8,128)(2,1)}, bf16[9,32,128]{2,1,0:T(8,128)(2,1)S(1)}) custom-call(s32[256]{0:T(256)S(1)} %copy-done.20, s32[12]{0:T(128)S(1)} %copy-done.25, bf16[192,32,128]{2,1,0:T(8,128)(2,1)} %bitcast.2.terms_ref, f32[8,32,256]{2,1,0:T(8,128)S(1)} %copy-done.12, bf16[8,96,256]{2,1,0:T(8,128)(2,1)S(1)} %copy-done.5, ...), custom_call_target="tpu_custom_call" | custom-call | tf_op jit(solution)/shard_map/pallas_call | solution.py:296
  135.5 20.4 %all_gather.21 = bf16[36,32,128]{2,1,0:T(8,128)(2,1)} all-gather(bf16[9,32,128]{2,1,0:T(8,128)(2,1)S(1)} %get-tuple-element.9), channel_id=1, replica_groups={{0,8,16,24},{1,9,17,25},{2,10,18,26},{3,11,19,27},{4,12,20,28},{5,13,21..., dimensions={0}, use_global_device_ids=true | all-gather | bytes 368640 | tf_op jit(solution)/shard_map/all_gather | solution.py:215
  155.8 0.0 all-gather.9.cloned.1.call-update
  155.9 0.0 all-gather.11.cloned.1.call-start
  155.9 24.3 %all-gather.9.cloned.1.call-done = bf16[144,32,128]{2,1,0:T(8,128)(2,1)} async-done(((bf16[36,32,128]{2,1,0:T(8,128)(2,1)}), bf16[144,32,128]{2,1,0:T(8,128)(2,1)}) %all-gather.9.cloned.1.call-update) | async-done | bytes 1179664 | tf_op jit(solution)/shard_map/all_gather | solution.py:215
  180.2 0.0 all-gather.11.cloned.1.call-update
  180.2 12.4 %all-gather.11.cloned.1.call-done.gathered_ref = bf16[288,32,128]{2,1,0:T(8,128)(2,1)} async-done(((bf16[144,32,128]{2,1,0:T(8,128)(2,1)}), bf16[288,32,128]{2,1,0:T(8,128)(2,1)}) %all-gather.11.cloned.1.call-update) | async-done | bytes 2359312 | tf_op jit(solution)/shard_map/all_gather | solution.py:215
  192.6 1.7 copy-done.7
  194.2 7.5 %shard_map.100 = bf16[192,32,128]{2,1,0:T(8,128)(2,1)S(1)} custom-call(s32[128]{0:T(128)S(1)} %copy-done.32, s32[128]{0:T(128)S(1)} %copy-done.23, s32[128]{0:T(128)S(1)} %copy-done.30, s32[128]{0:T(128)S(1)} %copy-done.28, bf16[288,32,128]{2,1,0:T(8,128)(2,1)S(1)} %copy-done.7, bf16[128,96,96]{2,1,0:T(8,128)(2,1)S(1)} %copy.15.coupling_ref), custom_call_target="tpu_custom_call" | custom-call | flops 75497472 | bytes 10485760 | tf_op jit(solution)/shard_map/pallas_call | solution.py:289
  201.8 1.1 copy-done.3
  202.9 5.9 %all-to-all-start.2 = ((bf16[32,6,32,128]{3,2,1,0:T(8,128)(2,1)}), bf16[32,6,32,128]{3,2,1,0:T(8,128)(2,1)}, u32[]{:S(2)}, u32[]{:S(2)}) async-start(bf16[32,6,32,128]{3,2,1,0:T(8,128)(2,1)} %bitcast.6), calls=%async_computation.2 | async-start | bytes 3145728 | tf_op jit(solution)/shard_map/all_to_all | solution.py:290
  208.8 0.7 fusion.5
  209.5 2.1 collective-permute-start.2
  211.6 0.0 copy-start.26
  211.6 1.3 collective-permute-start.3
  212.9 2.9 %collective-permute-done.3.after_ref = bf16[1,32,256]{2,1,0:T(8,128)(2,1)S(1)} collective-permute-done((bf16[1,32,256]{2,1,0:T(8,128)(2,1)S(1)}, bf16[1,32,256]{2,1,0:T(8,128)(2,1)S(1)}, u32[]{:S(2)}, u32[]{:S(2)}) %collective-permute-start.3) | collective-permute-done | bytes 16416 | tf_op jit(solution)/shard_map/ppermute | solution.py:294
  215.8 0.9 copy-done.17
  216.8 0.6 shard_map.101.near_ref
  217.4 0.7 copy-done.13
  218.1 28.4 %all-to-all-done.2 = bf16[32,6,32,128]{3,2,1,0:T(8,128)(2,1)} async-done(((bf16[32,6,32,128]{3,2,1,0:T(8,128)(2,1)}), bf16[32,6,32,128]{3,2,1,0:T(8,128)(2,1)}, u32[]{:S(2)}, u32[]{:S(2)}) %all-to-all-start.2) | async-done | bytes 1572896 | tf_op jit(solution)/shard_map/all_to_all | solution.py:290
  246.5 0.9 copy-done.10
  247.4 0.9 copy-done.14
  248.4 6.2 %shard_map.102 = bf16[8,32,256]{2,1,0:T(8,128)(2,1)} custom-call(s32[256]{0:T(256)S(1)} %copy-done.21, s32[12]{0:T(128)S(1)} %copy-done.26, bf16[192,32,128]{2,1,0:T(8,128)(2,1)} %bitcast.4.terms_ref, f32[8,32,256]{2,1,0:T(8,128)S(1)} %copy-done.14, bf16[8,96,256]{2,1,0:T(8,128)(2,1)S(1)} %copy-done.5, bf16[8,96,96]{2,1,0:T(8,128)(2,1)S(1)} %copy-done.10), custom_call_target="tpu_custom_call" | custom-call | tf_op jit(solution)/shard_map/pallas_call | solution.py:296
  (50 shorter events, 0.1 us)
Async XLA Ops:
  7.2 50.5 %all-gather.5.cloned.1.call-start = ((), (), s32[]{:S(2)}) async-start(), calls=%async_computation.3 | async-start | bytes 1474560 | tf_op jit(solution)/shard_map/all_gather | solution.py:215
  7.2 1.0 copy-start.4
  8.2 0.9 copy-start.8
  9.1 0.9 copy-start.15
  10.0 0.7 copy-start.24
  28.1 43.9 %all-gather.7.cloned.1.call-start = ((), (), s32[]{:S(2)}) async-start(), calls=%async_computation.4 | async-start | bytes 3538944 | tf_op jit(solution)/shard_map/all_gather | solution.py:215
  63.7 18.7 %all-to-all-start = ((s32[32,1,8]{2,1,0:T(1,128)}), s32[32,1,8]{2,1,0:T(1,128)S(1)}, u32[]{:S(2)}, u32[]{:S(2)}) async-start(s32[32,1,8]{2,1,0:T(1,128)} %bitcast), calls=%async_computation | async-start | bytes 32768 | tf_op jit(solution)/shard_map/all_to_all | solution.py:242
  68.3 3.6 %copy-start.33 = (s32[128]{0:T(128)S(1)}, s32[128]{0:T(128)}, u32[]{:S(2)}) copy-start(s32[128]{0:T(128)} %param.14) | copy-start | bytes 1540
  68.3 3.7 %copy-start.27 = (s32[128]{0:T(128)S(1)}, s32[128]{0:T(128)}, u32[]{:S(2)}) copy-start(s32[128]{0:T(128)} %get-tuple-element.7.slot_ref) | copy-start | bytes 1540
  71.9 9.3 %copy-start.29 = (s32[128]{0:T(128)}, s32[128]{0:T(128)S(1)}, u32[]{:S(2)}) copy-start(s32[128]{0:T(128)S(1)} %get-tuple-element.10.is_pad_ref) | copy-start | bytes 1540
  71.9 9.3 %copy-start.22 = (s32[128]{0:T(128)}, s32[128]{0:T(128)S(1)}, u32[]{:S(2)}) copy-start(s32[128]{0:T(128)S(1)} %get-tuple-element.12.pad_ref) | copy-start | bytes 1540
  72.0 9.3 %copy-start.31 = (s32[128]{0:T(128)}, s32[128]{0:T(128)S(1)}, u32[]{:S(2)}) copy-start(s32[128]{0:T(128)S(1)} %fusion.1.main_ref) | copy-start | bytes 1540
  72.0 1.7 copy-start.6
  81.2 1.1 copy-start.2
  82.4 43.7 %all-to-all-start.1 = ((bf16[32,6,32,128]{3,2,1,0:T(8,128)(2,1)}), bf16[32,6,32,128]{3,2,1,0:T(8,128)(2,1)}, u32[]{:S(2)}, u32[]{:S(2)}) async-start(bf16[32,6,32,128]{3,2,1,0:T(8,128)(2,1)} %bitcast.5), calls=%async_computation.1 | async-start | bytes 3145728 | tf_op jit(solution)/shard_map/all_to_all | solution.py:290
  88.3 91.8 %all-gather.9.cloned.1.call-start = ((), (), s32[]{:S(2)}) async-start(), calls=%async_computation.5 | async-start | bytes 1474560 | tf_op jit(solution)/shard_map/all_gather | solution.py:215
  89.1 5.3 %collective-permute-start = (bf16[1,32,256]{2,1,0:T(8,128)(2,1)S(1)}, bf16[1,32,256]{2,1,0:T(8,128)(2,1)S(1)}, u32[]{:S(2)}, u32[]{:S(2)}) collective-permute-start(bf16[1,32,256]{2,1,0:T(8,128)(2,1)S(1)} %get-tuple-element.17), channel_id=1, source_target_pairs={{0,1},{1,2},{2,3},{3,4},{4,5},{5,6},{6,7},{7,8},{8,9},{9,10},{10,1... | collective-permute-start | bytes 49160 | tf_op jit(solution)/shard_map/ppermute | solution.py:293
  91.2 4.2 %collective-permute-start.1 = (bf16[1,32,256]{2,1,0:T(8,128)(2,1)S(1)}, bf16[1,32,256]{2,1,0:T(8,128)(2,1)S(1)}, u32[]{:S(2)}, u32[]{:S(2)}) collective-permute-start(bf16[1,32,256]{2,1,0:T(8,128)(2,1)S(1)} %get-tuple-element.16), channel_id=1, source_target_pairs={{1,0},{2,1},{3,2},{4,3},{5,4},{6,5},{7,6},{8,7},{9,8},{10,9},{11,1... | collective-permute-start | bytes 49160 | tf_op jit(solution)/shard_map/ppermute | solution.py:294
  95.4 0.6 copy-start.18
  96.0 1.9 copy-start
  97.9 0.9 copy-start.16
  98.8 0.7 copy-start.19
  99.5 26.5 %copy-start.5 = (bf16[8,96,256]{2,1,0:T(8,128)(2,1)S(1)}, bf16[8,96,256]{2,1,0:T(8,128)(2,1)}, u32[]{:S(2)}) copy-start(bf16[8,96,256]{2,1,0:T(8,128)(2,1)} %basis_ref.5) | copy-start | bytes 1179652
  100.2 0.7 copy-start.11
  126.1 0.9 copy-start.9
  127.0 0.9 copy-start.12
  127.9 0.7 copy-start.20
  128.6 0.7 copy-start.25
  129.3 63.3 %copy-start.23 = (s32[128]{0:T(128)S(1)}, s32[128]{0:T(128)}, u32[]{:S(2)}) copy-start(s32[128]{0:T(128)} %copy-done.22) | copy-start | bytes 1540
  129.3 63.3 %copy-start.28 = (s32[128]{0:T(128)S(1)}, s32[128]{0:T(128)}, u32[]{:S(2)}) copy-start(s32[128]{0:T(128)} %get-tuple-element.7.slot_ref) | copy-start | bytes 1540
  129.3 63.3 %copy-start.30 = (s32[128]{0:T(128)S(1)}, s32[128]{0:T(128)}, u32[]{:S(2)}) copy-start(s32[128]{0:T(128)} %copy-done.29) | copy-start | bytes 1540
  129.3 63.3 %copy-start.32 = (s32[128]{0:T(128)S(1)}, s32[128]{0:T(128)}, u32[]{:S(2)}) copy-start(s32[128]{0:T(128)} %copy-done.31) | copy-start | bytes 1540
  155.9 36.7 %all-gather.11.cloned.1.call-start = ((), (), s32[]{:S(2)}) async-start(), calls=%async_computation.6 | async-start | bytes 3538944 | tf_op jit(solution)/shard_map/all_gather | solution.py:215
  192.6 1.7 copy-start.7
  201.8 1.1 copy-start.3
  202.9 13.0 %copy-start.1 = (bf16[8,3,256,256]{3,2,1,0:T(8,128)(2,1)S(1)}, bf16[8,3,256,256]{3,2,1,0:T(8,128)(2,1)}, u32[]{:S(2)}) copy-start(bf16[8,3,256,256]{3,2,1,0:T(8,128)(2,1)} %near_ref.3) | copy-start | bytes 9437188
  202.9 43.6 %all-to-all-start.2 = ((bf16[32,6,32,128]{3,2,1,0:T(8,128)(2,1)}), bf16[32,6,32,128]{3,2,1,0:T(8,128)(2,1)}, u32[]{:S(2)}, u32[]{:S(2)}) async-start(bf16[32,6,32,128]{3,2,1,0:T(8,128)(2,1)} %bitcast.6), calls=%async_computation.2 | async-start | bytes 3145728 | tf_op jit(solution)/shard_map/all_to_all | solution.py:290
  209.5 3.4 %collective-permute-start.2 = (bf16[1,32,256]{2,1,0:T(8,128)(2,1)S(1)}, bf16[1,32,256]{2,1,0:T(8,128)(2,1)S(1)}, u32[]{:S(2)}, u32[]{:S(2)}) collective-permute-start(bf16[1,32,256]{2,1,0:T(8,128)(2,1)S(1)} %get-tuple-element.15), channel_id=1, source_target_pairs={{0,1},{1,2},{2,3},{3,4},{4,5},{5,6},{6,7},{7,8},{8,9},{9,10},{10,1... | collective-permute-start | bytes 49160 | tf_op jit(solution)/shard_map/ppermute | solution.py:293
  211.6 34.9 %copy-start.21 = (s32[256]{0:T(256)S(1)}, s32[256]{0:T(256)}, u32[]{:S(2)}) copy-start(s32[256]{0:T(256)} %reshape.24.ids_ref) | copy-start | bytes 3076
  211.6 34.9 %copy-start.26 = (s32[12]{0:T(128)S(1)}, s32[12]{0:T(128)}, u32[]{:S(2)}) copy-start(s32[12]{0:T(128)} %ranks_ref.5) | copy-start | bytes 148
  211.6 4.2 %collective-permute-start.3 = (bf16[1,32,256]{2,1,0:T(8,128)(2,1)S(1)}, bf16[1,32,256]{2,1,0:T(8,128)(2,1)S(1)}, u32[]{:S(2)}, u32[]{:S(2)}) collective-permute-start(bf16[1,32,256]{2,1,0:T(8,128)(2,1)S(1)} %get-tuple-element.14), channel_id=1, source_target_pairs={{1,0},{2,1},{3,2},{4,3},{5,4},{6,5},{7,6},{8,7},{9,8},{10,9},{11,1... | collective-permute-start | bytes 49160 | tf_op jit(solution)/shard_map/ppermute | solution.py:294
  215.8 0.9 copy-start.17
  217.4 0.7 copy-start.13
  246.5 0.9 copy-start.10
  247.4 0.9 copy-start.14
Sparse Core Ops, SparseCore 0:
  28.2 29.4 all-gather.4
  59.2 10.9 all-gather.6
  156.0 24.1 all-gather.8
  181.6 10.9 all-gather.10

commit v2 on v1

v2 whole, which is shorter than its diff:
```python
import functools

import jax
import jax.numpy as jnp
from jax import lax
from jax.experimental import pallas as pl
from jax.experimental.pallas import tpu as pltpu
from jax.sharding import PartitionSpec as P

LANES = 128
BF = jnp.bfloat16
F32 = jnp.float32
VMEM = pl.BlockSpec(memory_space=pltpu.VMEM)
SMEM = pl.BlockSpec(memory_space=pltpu.SMEM)


def dot(a, b):
    return lax.dot_general(a, b, (((1,), (0,)), ((), ())), preferred_element_type=F32)


def dot_t(a, b):
    return lax.dot_general(a, b, (((1,), (1,)), ((), ())), preferred_element_type=F32)


def spread(rank_top, piece):
    third = LANES - rank_top
    row = lax.broadcasted_iota(jnp.int32, (rank_top, LANES), 0)
    lane = lax.broadcasted_iota(jnp.int32, (rank_top, LANES), 1)
    hit = (lane - rank_top == row - third * piece) & (lane >= rank_top)
    return hit.astype(F32).astype(BF)


def collect(rank_top, piece):
    third = LANES - rank_top
    row = lax.broadcasted_iota(jnp.int32, (LANES, LANES), 0)
    lane = lax.broadcasted_iota(jnp.int32, (LANES, LANES), 1)
    hit = (row - rank_top == lane - third * piece) & (row >= rank_top)
    return hit.astype(F32).astype(BF)


def emit_coeffs(read_leaf, basis_ref, transfer_ref, ranks_ref, out_ref, leaves, rank_top):
    copies, mains, rhs, _ = out_ref.shape
    lane = lax.broadcasted_iota(jnp.int32, (rhs, rank_top), 1)
    coeffs = []
    for i in range(leaves):
        value = dot_t(read_leaf(i), basis_ref[i])
        coeffs.append(jnp.where(lane < ranks_ref[i], value, 0.0).astype(BF))
    for q in range(leaves // 2):
        value = dot(coeffs[2 * q], transfer_ref[2 * q]) + dot(coeffs[2 * q + 1], transfer_ref[2 * q + 1])
        coeffs.append(jnp.where(lane < ranks_ref[leaves + q], value, 0.0).astype(BF))
    for q in range(mains // 3):
        for k in range(3):
            tile = dot(coeffs[mains + q], spread(rank_top, k)).astype(BF)
            for c in range(copies):
                out_ref[c, 3 * q + k] = tile
                out_ref[c, 3 * q + k, :, :rank_top] = coeffs[3 * q + k]


def coeff_kernel(ranks_ref, v_ref, basis_ref, transfer_ref, out_ref):
    leaves, rank_top, _ = basis_ref.shape
    emit_coeffs(lambda i: v_ref[i], basis_ref, transfer_ref, ranks_ref, out_ref, leaves, rank_top)


def couple_kernel(source_ref, target_ref, own_ref, other_ref, coupling_ref, keep_ref, send_ref, sources, total, *, unroll):
    blocks, rank_top, _ = coupling_ref.shape
    devices, mains, rhs, _ = own_ref.shape
    quads = mains // 3
    clusters = mains + quads
    gathers = [collect(rank_top, k) for k in range(3)]

    for half, packed_ref in enumerate((own_ref, other_ref)):

        def split(d, _):
            row = (half * devices + d) * clusters
            pads = None
            for k in range(3):
                tiles = jnp.concatenate([packed_ref[d, 3 * q + k] for q in range(quads)], axis=0)
                part = dot(tiles, gathers[k])
                pads = part if pads is None else pads + part
            pads = pads.astype(BF).reshape(quads, rhs, LANES)
            for c in range(mains):
                sources[row + c] = packed_ref[d, c]
            for q in range(quads):
                sources[row + mains + q] = pads[q]
            return 0

        lax.fori_loop(0, devices, split, 0)

    def clear(s, _):
        for u in range(clusters):
            total[s * clusters + u] = jnp.zeros((rhs, LANES), F32)
        return 0

    lax.fori_loop(0, 2 * devices, clear, 0)

    def some(s, _):
        for u in range(unroll):
            j = s * unroll + u
            term = dot(sources[source_ref[j], :, :rank_top], coupling_ref[j])
            at = target_ref[j]
            total[at, :, :rank_top] = total[at, :, :rank_top] + term
        return 0

    lax.fori_loop(0, blocks // unroll, some, 0)

    moves = [spread(rank_top, k) for k in range(3)]
    low = lax.broadcasted_iota(jnp.int32, (rhs, LANES), 1) < rank_top
    for half, packed_ref in enumerate((keep_ref, send_ref)):

        def pack(d, _):
            row = (half * devices + d) * clusters
            pads = jnp.concatenate([total[row + mains + q, :, :rank_top] for q in range(quads)], axis=0).astype(BF)
            for k in range(3):
                moved = dot(pads, moves[k]).reshape(quads, rhs, LANES)
                for q in range(quads):
                    packed_ref[d, 3 * q + k] = jnp.where(low, total[row + 3 * q + k], moved[q]).astype(BF)
            return 0

        lax.fori_loop(0, devices, pack, 0)


def near_kernel(v_ref, before_ref, after_ref, near_ref, out_ref):
    leaves = v_ref.shape[0]
    for i in range(leaves):
        left = v_ref[i - 1] if i > 0 else before_ref[0]
        right = v_ref[i + 1] if i < leaves - 1 else after_ref[0]
        out_ref[i] = dot(left, near_ref[i, 0]) + dot(v_ref[i], near_ref[i, 1]) + dot(right, near_ref[i, 2])


def field_kernel(ranks_ref, terms_ref, near_ref, basis_ref, transfer_ref, out_ref, *coeff_ref):
    leaves, rank_top, _ = basis_ref.shape
    parts, mains, rhs, _ = terms_ref.shape
    packed = []
    for t in range(mains):
        tile = terms_ref[0, t].astype(F32)
        for p in range(1, parts):
            tile = tile + terms_ref[p, t].astype(F32)
        packed.append(tile.astype(BF))
    sums = [tile[:, :rank_top] for tile in packed]
    for q in range(mains // 3):
        pad = None
        for k in range(3):
            part = dot(packed[3 * q + k], collect(rank_top, k))
            pad = part if pad is None else pad + part
        sums.append(pad[:, :rank_top].astype(BF))
    lane = lax.broadcasted_iota(jnp.int32, (rhs, rank_top), 1)
    fields = [jnp.where(lane < ranks_ref[c], total.astype(F32), 0.0) for c, total in enumerate(sums)]
    for i in range(leaves):
        down = fields[i] + dot_t(fields[leaves + i // 2].astype(BF), transfer_ref[i])
        leaf_total = jnp.where(lane < ranks_ref[i], down, 0.0).astype(BF)
        out_ref[i] = (near_ref[i] + dot(leaf_total, basis_ref[i])).astype(BF)
    if coeff_ref:
        emit_coeffs(lambda i: out_ref[i], basis_ref, transfer_ref, ranks_ref, coeff_ref[0], leaves, rank_top)


def params(mebibytes):
    return pltpu.CompilerParams(vmem_limit_bytes=mebibytes << 20)


def local(charges, basis, transfer, near_field, coupling, ranks, block_source, block_target):
    leaves, rank_top, width = basis.shape
    rhs = charges.shape[1]
    clusters = ranks.shape[0]
    blocks = coupling.shape[0]
    devices = lax.axis_size("clu")
    mains = clusters * 3 // 4
    shape = jax.ShapeDtypeStruct

    cores, chips = 2, 4
    planes = devices // (cores * chips)
    half = chips * planes
    plane_groups = [[p * cores * chips + r for p in range(planes)] for r in range(cores * chips)]
    chip_groups = [
        [p * cores * chips + c * cores + k for c in range(chips)] for p in range(planes) for k in range(cores)
    ]

    def exchange(parts, groups):
        return lax.all_to_all(
            parts, "clu", split_axis=0, concat_axis=0, tiled=True, axis_index_groups=groups
        )

    def swap_cores(part):
        return lax.ppermute(part, "clu", [(d, d ^ 1) for d in range(devices)])

    core = lax.axis_index("clu") % cores

    def rows(cluster):
        device = cluster // clusters
        chip, plane = (device // cores) % chips, device // (cores * chips)
        return (((device % cores + core) % cores * chips + chip) * planes + plane) * clusters + cluster % clusters

    source_rows, target_rows = rows(block_source), rows(block_target)

    coeff_shape = shape((planes, mains, rhs, LANES), BF)
    out_shape = shape((leaves, rhs, width), BF)
    half_shape = shape((half, mains, rhs, LANES), BF)
    first_coeffs = pl.pallas_call(
        coeff_kernel,
        out_shape=coeff_shape,
        in_specs=[SMEM, VMEM, VMEM, VMEM],
        out_specs=VMEM,
        compiler_params=params(16),
    )(ranks, charges, basis, transfer)

    couple = pl.pallas_call(
        functools.partial(couple_kernel, unroll=8),
        out_shape=[half_shape, half_shape],
        in_specs=[SMEM, SMEM, VMEM, VMEM, VMEM],
        out_specs=[VMEM, VMEM],
        scratch_shapes=[
            pltpu.VMEM((devices * clusters, rhs, LANES), BF),
            pltpu.VMEM((devices * clusters, rhs, LANES), F32),
        ],
        compiler_params=params(32 if devices <= 32 else 60),
        cost_estimate=pl.CostEstimate(
            flops=2 * blocks * rhs * rank_top * rank_top, bytes_accessed=10 << 20, transcendentals=0
        ),
    )

    near = pl.pallas_call(
        near_kernel,
        out_shape=shape((leaves, rhs, width), F32),
        in_specs=[VMEM] * 4,
        out_specs=VMEM,
        compiler_params=params(16),
        cost_estimate=pl.CostEstimate(
            flops=2 * leaves * 3 * rhs * width * width, bytes_accessed=4 << 20, transcendentals=0
        ),
    )

    def finish(with_coeffs):
        return pl.pallas_call(
            field_kernel,
            out_shape=[out_shape, coeff_shape] if with_coeffs else [out_shape],
            in_specs=[SMEM, VMEM, VMEM, VMEM, VMEM],
            out_specs=[VMEM, VMEM] if with_coeffs else [VMEM],
            compiler_params=params(16),
        )

    ends = devices - 1

    def apply_matrix(field_in, coeffs, with_coeffs):
        column = exchange(coeffs, plane_groups)
        own = exchange(jnp.broadcast_to(column[None], (chips,) + column.shape), chip_groups)
        own = own.reshape(half_shape.shape)
        other = swap_cores(own)
        keep, send = couple(source_rows, target_rows, own, other, coupling)
        chip_sum = keep.astype(F32) + swap_cores(send).astype(F32)
        parts = exchange(chip_sum.astype(BF).reshape(chips, planes, mains, rhs, LANES), chip_groups)
        column_sum = jnp.sum(parts.astype(F32), axis=0).astype(BF)
        terms = exchange(column_sum, plane_groups)
        before = lax.ppermute(field_in[leaves - 1 :], "clu", [(i, i + 1) for i in range(ends)])
        after = lax.ppermute(field_in[:1], "clu", [(i + 1, i) for i in range(ends)])
        near_sum = near(field_in, before, after, near_field)
        return finish(with_coeffs)(ranks, terms, near_sum, basis, transfer)

    first, second_coeffs = apply_matrix(charges, first_coeffs, True)
    (second,) = apply_matrix(first, second_coeffs, False)
    return (first, second)


def solution(mesh):
    in_specs = (
        P("clu", None, None),
        P("clu", None, None),
        P("clu", None, None),
        P("clu", None, None, None),
        P("clu", None, None),
        P("clu"),
        P("clu"),
        P("clu"),
    )
    out_specs = (P("clu", None, None), P("clu", None, None))
    return jax.shard_map(local, mesh=mesh, in_specs=in_specs, out_specs=out_specs, check_vma=False)
```

time: 263 us -> 201 us (0.76)
  the two profiles are of different devices: /device:TPU:0 before, /device:TPU:7 now
where the time goes in v2:
time: 201 us; the launch traced here: 200 us
  blocking collectives  90.3 us (45%)
  Pallas kernels  37.3 us (19%)
  starting transfers between devices  30.7 us (15%)
  local copies, waits for them, and re-layouts  17.8 us (9%)
  waiting for transfers between devices  17.6 us (9%)
  other arithmetic  5.11 us (3%)
    all_to_all x6, blocking collectives, exchange(): lax.all_to_all(parts, 'clu', split_axis=0, concat_axis=0, tiled=True, axi...  90.3 us
    pallas_call x2, Pallas kernels, apply_matrix(): keep, send = couple(source_rows, target_rows, own, other, coupling)  29 us
    unnamed x37, local copies, waits for them, and re-layouts  15.9 us
    ppermute x2, starting transfers between devices, apply_matrix(): lax.ppermute(field_in[leaves - 1:], 'clu', [(i, i + 1) for i in range(end...  12.1 us
    ppermute x2, waiting for transfers between devices, apply_matrix(): after = lax.ppermute(field_in[:1], 'clu', [(i + 1, i) for i in range(ends)])  9.83 us
    all_to_all x2, starting transfers between devices, exchange(): lax.all_to_all(parts, 'clu', split_axis=0, concat_axis=0, tiled=True, axi...  8.18 us
    ppermute x4, waiting for transfers between devices, swap_cores(): return lax.ppermute(part, 'clu', [(d, d ^ 1) for d in range(devices)])  7.79 us
    ppermute x4, starting transfers between devices, swap_cores(): return lax.ppermute(part, 'clu', [(d, d ^ 1) for d in range(devices)])  6.57 us
  transfers between devices with their start and end apart: 10, of which 5 were waited for; matrix products, arithmetic and copies ran while one was open for 3% of the time, Pallas kernels for 1%

profile of v2, /device:TPU:7, one launch (start us, length us, event | category | flops | bytes accessed | tf_op | source)
XLA Modules:
  0.0 199.6 jit_solution(15672196628161268272)
XLA Ops:
  0.6 0.0 copy-start.2
  0.6 1.0 copy-done.2
  1.6 0.9 copy-done.4
  2.6 0.9 copy-done.11
  3.5 0.7 copy-done.14
  4.1 1.0 shard_map.95
  5.2 12.2 %all_to_all.40 = bf16[4,9,32,128]{3,2,1,0:T(8,128)(2,1)S(1)} all-to-all(bf16[4,9,32,128]{3,2,1,0:T(8,128)(2,1)S(1)} %shard_map.95), channel_id=1, replica_groups={{0,8,16,24},{1,9,17,25},{2,10,18,26},{3,11,19,27},{4,12,20,28},{5,13,21..., dimensions={0} | all-to-all | bytes 589824 | tf_op jit(solution)/shard_map/all_to_all | solution.py:178
  17.4 0.2 broadcast_in_dim.4
  17.6 14.3 %all_to_all.41 = bf16[4,4,9,32,128]{4,3,2,1,0:T(8,128)(2,1)} all-to-all(bf16[4,4,9,32,128]{4,3,2,1,0:T(8,128)(2,1)S(1)} %broadcast_in_dim.4), channel_id=1, replica_groups={{0,2,4,6},{1,3,5,7},{8,10,12,14},{9,11,13,15},{16,18,20,22},{17,19,21,2..., dimensions={0} | all-to-all | bytes 2359296 | tf_op jit(solution)/shard_map/all_to_all | solution.py:178
  31.9 4.0 %collective-permute-start = (bf16[16,9,32,128]{3,2,1,0:T(8,128)(2,1)}, bf16[16,9,32,128]{3,2,1,0:T(8,128)(2,1)}, u32[]{:S(2)}, u32[]{:S(2)}) collective-permute-start(bf16[16,9,32,128]{3,2,1,0:T(8,128)(2,1)} %bitcast.own_ref), channel_id=1, source_target_pairs={{0,1},{1,0},{2,3},{3,2},{4,5},{5,4},{6,7},{7,6},{8,9},{9,8},{10,11... | collective-permute-start | bytes 3538952 | tf_op jit(solution)/shard_map/ppermute | solution.py:183
  35.9 3.6 %copy.10.coupling_ref = bf16[128,96,96]{2,1,0:T(8,128)(2,1)S(1)} copy(bf16[128,96,96]{0,2,1:T(8,128)(2,1)} %param.12) | data formatting | bytes 4718592 | tf_op args[4]
  39.5 0.0 copy-done.16
  39.5 0.0 copy-done.17
  39.5 0.0 collective-permute-done.other_ref
  39.5 15.1 %shard_map.96 = (bf16[16,9,32,128]{3,2,1,0:T(8,128)(2,1)S(1)}, bf16[16,9,32,128]{3,2,1,0:T(8,128)(2,1)S(1)}) custom-call(s32[128]{0:T(128)S(1)} %get-tuple-element.18.source_ref, s32[128]{0:T(128)S(1)} %get-tuple-element.19.target_ref, bf16[16,9,32,128]{3,2,1,0:T(8,128)(2,1)} %bitcast.own_ref, bf16[16,9,32,128]{3,2,1,0:T(8,128)(2,1)} %collective-permute-done.other_ref, ...), custom_call_target="tpu_custom_call" | custom-call | flops 75497472 | bytes 10485760 | tf_op jit(solution)/shard_map/pallas_call | solution.py:247
  54.6 0.1 collective-permute-start.1
  54.7 2.8 %collective-permute-done.1 = bf16[16,9,32,128]{3,2,1,0:T(8,128)(2,1)S(1)} collective-permute-done((bf16[16,9,32,128]{3,2,1,0:T(8,128)(2,1)S(1)}, bf16[16,9,32,128]{3,2,1,0:T(8,128)(2,1)S(1)}, u32[]{:S(2)}, u32[]{:S(2)}) %collective-permute-start.1) | collective-permute-done | bytes 1179680 | tf_op jit(solution)/shard_map/ppermute | solution.py:183
  57.5 0.3 add_convert_fusion.1
  57.8 18.7 %all_to_all.42 = bf16[4,4,9,32,128]{4,3,2,1,0:T(8,128)(2,1)} all-to-all(bf16[4,4,9,32,128]{4,3,2,1,0:T(8,128)(2,1)S(1)} %bitcast.6), channel_id=1, replica_groups={{0,2,4,6},{1,3,5,7},{8,10,12,14},{9,11,13,15},{16,18,20,22},{17,19,21,2..., dimensions={0} | all-to-all | bytes 2359296 | tf_op jit(solution)/shard_map/all_to_all | solution.py:178
  76.5 2.2 %reduce_sum.24 = bf16[4,9,32,128]{3,2,1,0:T(8,128)(2,1)} reduce(bf16[4,4,9,32,128]{4,3,2,1,0:T(8,128)(2,1)} %all_to_all.42, bf16[]{:T(256)} %constant.114.clone.1), dimensions={0}, to_apply=%region_0.1 | reduce | flops 442368 | bytes 1474562 | tf_op jit(solution)/shard_map/reduce_sum | solution.py:250
  78.7 4.1 %all-to-all-start.3 = ((bf16[4,9,32,128]{3,2,1,0:T(8,128)(2,1)}), bf16[4,9,32,128]{3,2,1,0:T(8,128)(2,1)}, u32[]{:S(2)}, u32[]{:S(2)}) async-start(bf16[4,9,32,128]{3,2,1,0:T(8,128)(2,1)} %reduce_sum.24), calls=%async_computation.3 | async-start | bytes 589824 | tf_op jit(solution)/shard_map/all_to_all | solution.py:178
  82.8 0.7 fusion.13
  83.6 5.9 %collective-permute-start.2 = (bf16[1,32,256]{2,1,0:T(8,128)(2,1)S(1)}, bf16[1,32,256]{2,1,0:T(8,128)(2,1)S(1)}, u32[]{:S(2)}, u32[]{:S(2)}) collective-permute-start(bf16[1,32,256]{2,1,0:T(8,128)(2,1)S(1)} %get-tuple-element.17), channel_id=1, source_target_pairs={{0,1},{1,2},{2,3},{3,4},{4,5},{5,6},{6,7},{7,8},{8,9},{9,10},{10,1... | collective-permute-start | bytes 49160 | tf_op jit(solution)/shard_map/ppermute | solution.py:252
  89.5 0.0 copy-start.15
  89.5 1.9 collective-permute-start.3
  91.4 0.0 collective-permute-done.2.before_ref
  91.4 4.9 %collective-permute-done.3.after_ref = bf16[1,32,256]{2,1,0:T(8,128)(2,1)S(1)} collective-permute-done((bf16[1,32,256]{2,1,0:T(8,128)(2,1)S(1)}, bf16[1,32,256]{2,1,0:T(8,128)(2,1)S(1)}, u32[]{:S(2)}, u32[]{:S(2)}) %collective-permute-start.3) | collective-permute-done | bytes 16416 | tf_op jit(solution)/shard_map/ppermute | solution.py:253
  96.3 1.9 copy-done
  98.2 0.9 copy-done.12
  99.1 0.6 shard_map.97.near_ref
  99.8 0.7 copy-done.7
  100.5 0.0 all-to-all-done.3.terms_ref
  100.5 0.0 copy-done.15
  100.5 0.0 copy-done.3
  100.5 0.0 copy-start.5
  100.5 0.9 copy-done.5
  101.4 0.9 copy-done.8
  102.4 3.0 %shard_map.98 = (bf16[8,32,256]{2,1,0:T(8,128)(2,1)}, bf16[4,9,32,128]{3,2,1,0:T(8,128)(2,1)S(1)}) custom-call(s32[12]{0:T(128)S(1)} %copy-done.15, bf16[4,9,32,128]{3,2,1,0:T(8,128)(2,1)} %all-to-all-done.3.terms_ref, f32[8,32,256]{2,1,0:T(8,128)S(1)} %copy-done.8, bf16[8,96,256]{2,1,0:T(8,128)(2,1)S(1)} %copy-done.3, bf16[8,96,96]{2,1,0:T(8,128)(2,1)S(1)} %copy-done.5), custom_call_target="tpu_custom_call" | custom-call | tf_op jit(solution)/shard_map/pallas_call | solution.py:255
  105.4 10.3 %all_to_all.43 = bf16[4,9,32,128]{3,2,1,0:T(8,128)(2,1)S(1)} all-to-all(bf16[4,9,32,128]{3,2,1,0:T(8,128)(2,1)S(1)} %get-tuple-element.11), channel_id=1, replica_groups={{0,8,16,24},{1,9,17,25},{2,10,18,26},{3,11,19,27},{4,12,20,28},{5,13,21..., dimensions={0} | all-to-all | bytes 589824 | tf_op jit(solution)/shard_map/all_to_all | solution.py:178
  115.7 0.2 broadcast_in_dim.5
  115.9 16.1 %all_to_all.44 = bf16[4,4,9,32,128]{4,3,2,1,0:T(8,128)(2,1)S(1)} all-to-all(bf16[4,4,9,32,128]{4,3,2,1,0:T(8,128)(2,1)S(1)} %broadcast_in_dim.5), channel_id=1, replica_groups={{0,2,4,6},{1,3,5,7},{8,10,12,14},{9,11,13,15},{16,18,20,22},{17,19,21,2..., dimensions={0} | all-to-all | bytes 2359296 | tf_op jit(solution)/shard_map/all_to_all | solution.py:178
  132.0 2.1 %collective-permute-start.4 = (bf16[16,9,32,128]{3,2,1,0:T(8,128)(2,1)S(1)}, bf16[16,9,32,128]{3,2,1,0:T(8,128)(2,1)S(1)}, u32[]{:S(2)}, u32[]{:S(2)}) collective-permute-start(bf16[16,9,32,128]{3,2,1,0:T(8,128)(2,1)S(1)} %bitcast.4), channel_id=1, source_target_pairs={{0,1},{1,0},{2,3},{3,2},{4,5},{5,4},{6,7},{7,6},{8,9},{9,8},{10,11... | collective-permute-start | bytes 3538952 | tf_op jit(solution)/shard_map/ppermute | solution.py:183
  134.1 2.5 %collective-permute-done.4.other_ref = bf16[16,9,32,128]{3,2,1,0:T(8,128)(2,1)S(1)} collective-permute-done((bf16[16,9,32,128]{3,2,1,0:T(8,128)(2,1)S(1)}, bf16[16,9,32,128]{3,2,1,0:T(8,128)(2,1)S(1)}, u32[]{:S(2)}, u32[]{:S(2)}) %collective-permute-start.4) | collective-permute-done | bytes 1179680 | tf_op jit(solution)/shard_map/ppermute | solution.py:183
  136.6 14.0 %shard_map.99 = (bf16[16,9,32,128]{3,2,1,0:T(8,128)(2,1)S(1)}, bf16[16,9,32,128]{3,2,1,0:T(8,128)(2,1)S(1)}) custom-call(s32[128]{0:T(128)S(1)} %get-tuple-element.18.source_ref, s32[128]{0:T(128)S(1)} %get-tuple-element.19.target_ref, bf16[16,9,32,128]{3,2,1,0:T(8,128)(2,1)S(1)} %bitcast.5, bf16[16,9,32,128]{3,2,1,0:T(8,128)(2,1)S(1)} %collective-permute-done.4.other_ref, ...), custom_call_target="tpu_custom_call" | custom-call | flops 75497472 | bytes 10485760 | tf_op jit(solution)/shard_map/pallas_call | solution.py:247
  150.6 0.4 collective-permute-start.5
  151.0 2.5 %collective-permute-done.5 = bf16[16,9,32,128]{3,2,1,0:T(8,128)(2,1)S(1)} collective-permute-done((bf16[16,9,32,128]{3,2,1,0:T(8,128)(2,1)S(1)}, bf16[16,9,32,128]{3,2,1,0:T(8,128)(2,1)S(1)}, u32[]{:S(2)}, u32[]{:S(2)}) %collective-permute-start.5) | collective-permute-done | bytes 1179680 | tf_op jit(solution)/shard_map/ppermute | solution.py:183
  153.5 0.3 add_convert_fusion
  153.8 0.0 copy-start.1
  153.8 18.6 %all_to_all.45 = bf16[4,4,9,32,128]{4,3,2,1,0:T(8,128)(2,1)} all-to-all(bf16[4,4,9,32,128]{4,3,2,1,0:T(8,128)(2,1)S(1)} %bitcast.7), channel_id=1, replica_groups={{0,2,4,6},{1,3,5,7},{8,10,12,14},{9,11,13,15},{16,18,20,22},{17,19,21,2..., dimensions={0} | all-to-all | bytes 2359296 | tf_op jit(solution)/shard_map/all_to_all | solution.py:178
  172.4 2.2 %reduce_sum.25 = bf16[4,9,32,128]{3,2,1,0:T(8,128)(2,1)} reduce(bf16[4,4,9,32,128]{4,3,2,1,0:T(8,128)(2,1)} %all_to_all.45, bf16[]{:T(256)} %constant.114.clone.1), dimensions={0}, to_apply=%region_1.2 | reduce | flops 442368 | bytes 1474562 | tf_op jit(solution)/shard_map/reduce_sum | solution.py:250
  174.7 4.1 %all-to-all-start.7 = ((bf16[4,9,32,128]{3,2,1,0:T(8,128)(2,1)}), bf16[4,9,32,128]{3,2,1,0:T(8,128)(2,1)}, u32[]{:S(2)}, u32[]{:S(2)}) async-start(bf16[4,9,32,128]{3,2,1,0:T(8,128)(2,1)} %reduce_sum.25), calls=%async_computation.7 | async-start | bytes 589824 | tf_op jit(solution)/shard_map/all_to_all | solution.py:178
  178.8 0.7 fusion.12
  179.5 6.2 %collective-permute-start.6 = (bf16[1,32,256]{2,1,0:T(8,128)(2,1)S(1)}, bf16[1,32,256]{2,1,0:T(8,128)(2,1)S(1)}, u32[]{:S(2)}, u32[]{:S(2)}) collective-permute-start(bf16[1,32,256]{2,1,0:T(8,128)(2,1)S(1)} %get-tuple-element.15), channel_id=1, source_target_pairs={{0,1},{1,2},{2,3},{3,4},{4,5},{5,6},{6,7},{7,8},{8,9},{9,10},{10,1... | collective-permute-start | bytes 49160 | tf_op jit(solution)/shard_map/ppermute | solution.py:252
  185.7 1.9 collective-permute-start.7
  187.6 0.0 collective-permute-done.6.before_ref
  187.6 4.9 %collective-permute-done.7.after_ref = bf16[1,32,256]{2,1,0:T(8,128)(2,1)S(1)} collective-permute-done((bf16[1,32,256]{2,1,0:T(8,128)(2,1)S(1)}, bf16[1,32,256]{2,1,0:T(8,128)(2,1)S(1)}, u32[]{:S(2)}, u32[]{:S(2)}) %collective-permute-start.7) | collective-permute-done | bytes 16416 | tf_op jit(solution)/shard_map/ppermute | solution.py:253
  192.6 0.0 copy-done.1
  192.6 0.9 copy-done.13
  193.5 0.6 shard_map.100.near_ref
  194.1 0.7 copy-done.9
  194.8 0.0 all-to-all-done.7.terms_ref
  194.8 0.9 copy-done.6
  195.8 0.9 copy-done.10
  196.7 2.9 %shard_map.101 = bf16[8,32,256]{2,1,0:T(8,128)(2,1)} custom-call(s32[12]{0:T(128)S(1)} %copy-done.15, bf16[4,9,32,128]{3,2,1,0:T(8,128)(2,1)} %all-to-all-done.7.terms_ref, f32[8,32,256]{2,1,0:T(8,128)S(1)} %copy-done.10, bf16[8,96,256]{2,1,0:T(8,128)(2,1)S(1)} %copy-done.3, bf16[8,96,96]{2,1,0:T(8,128)(2,1)S(1)} %copy-done.6), custom_call_target="tpu_custom_call" | custom-call | tf_op jit(solution)/shard_map/pallas_call | solution.py:255
  (15 shorter events, 0.1 us)
Async XLA Ops:
  0.6 1.0 copy-start.2
  1.6 0.9 copy-start.4
  2.6 0.9 copy-start.11
  3.5 0.7 copy-start.14
  31.9 7.6 %collective-permute-start = (bf16[16,9,32,128]{3,2,1,0:T(8,128)(2,1)}, bf16[16,9,32,128]{3,2,1,0:T(8,128)(2,1)}, u32[]{:S(2)}, u32[]{:S(2)}) collective-permute-start(bf16[16,9,32,128]{3,2,1,0:T(8,128)(2,1)} %bitcast.own_ref), channel_id=1, source_target_pairs={{0,1},{1,0},{2,3},{3,2},{4,5},{5,4},{6,7},{7,6},{8,9},{9,8},{10,11... | collective-permute-start | bytes 3538952 | tf_op jit(solution)/shard_map/ppermute | solution.py:183
  35.9 3.6 %copy-start.16 = (s32[128]{0:T(128)S(1)}, s32[128]{0:T(128)}, u32[]{:S(2)}) copy-start(s32[128]{0:T(128)} %param.14) | copy-start | bytes 1540
  35.9 3.6 %copy-start.17 = (s32[128]{0:T(128)S(1)}, s32[128]{0:T(128)}, u32[]{:S(2)}) copy-start(s32[128]{0:T(128)} %param.15) | copy-start | bytes 1540
  54.6 2.9 %collective-permute-start.1 = (bf16[16,9,32,128]{3,2,1,0:T(8,128)(2,1)S(1)}, bf16[16,9,32,128]{3,2,1,0:T(8,128)(2,1)S(1)}, u32[]{:S(2)}, u32[]{:S(2)}) collective-permute-start(bf16[16,9,32,128]{3,2,1,0:T(8,128)(2,1)S(1)} %get-tuple-element.9), channel_id=1, source_target_pairs={{0,1},{1,0},{2,3},{3,2},{4,5},{5,4},{6,7},{7,6},{8,9},{9,8},{10,11... | collective-permute-start | bytes 3538952 | tf_op jit(solution)/shard_map/ppermute | solution.py:183
  78.7 21.8 %all-to-all-start.3 = ((bf16[4,9,32,128]{3,2,1,0:T(8,128)(2,1)}), bf16[4,9,32,128]{3,2,1,0:T(8,128)(2,1)}, u32[]{:S(2)}, u32[]{:S(2)}) async-start(bf16[4,9,32,128]{3,2,1,0:T(8,128)(2,1)} %reduce_sum.24), calls=%async_computation.3 | async-start | bytes 589824 | tf_op jit(solution)/shard_map/all_to_all | solution.py:178
  83.6 7.9 %collective-permute-start.2 = (bf16[1,32,256]{2,1,0:T(8,128)(2,1)S(1)}, bf16[1,32,256]{2,1,0:T(8,128)(2,1)S(1)}, u32[]{:S(2)}, u32[]{:S(2)}) collective-permute-start(bf16[1,32,256]{2,1,0:T(8,128)(2,1)S(1)} %get-tuple-element.17), channel_id=1, source_target_pairs={{0,1},{1,2},{2,3},{3,4},{4,5},{5,6},{6,7},{7,8},{8,9},{9,10},{10,1... | collective-permute-start | bytes 49160 | tf_op jit(solution)/shard_map/ppermute | solution.py:252
  89.5 11.0 %copy-start.15 = (s32[12]{0:T(128)S(1)}, s32[12]{0:T(128)}, u32[]{:S(2)}) copy-start(s32[12]{0:T(128)} %ranks_ref.5) | copy-start | bytes 148
  89.5 6.9 %collective-permute-start.3 = (bf16[1,32,256]{2,1,0:T(8,128)(2,1)S(1)}, bf16[1,32,256]{2,1,0:T(8,128)(2,1)S(1)}, u32[]{:S(2)}, u32[]{:S(2)}) collective-permute-start(bf16[1,32,256]{2,1,0:T(8,128)(2,1)S(1)} %get-tuple-element.16), channel_id=1, source_target_pairs={{1,0},{2,1},{3,2},{4,3},{5,4},{6,5},{7,6},{8,7},{9,8},{10,9},{11,1... | collective-permute-start | bytes 49160 | tf_op jit(solution)/shard_map/ppermute | solution.py:253
  96.3 1.9 copy-start
  98.2 0.9 copy-start.12
  99.1 1.4 copy-start.3
  99.8 0.7 copy-start.7
  100.5 0.9 copy-start.5
  101.4 0.9 copy-start.8
  132.0 4.6 %collective-permute-start.4 = (bf16[16,9,32,128]{3,2,1,0:T(8,128)(2,1)S(1)}, bf16[16,9,32,128]{3,2,1,0:T(8,128)(2,1)S(1)}, u32[]{:S(2)}, u32[]{:S(2)}) collective-permute-start(bf16[16,9,32,128]{3,2,1,0:T(8,128)(2,1)S(1)} %bitcast.4), channel_id=1, source_target_pairs={{0,1},{1,0},{2,3},{3,2},{4,5},{5,4},{6,7},{7,6},{8,9},{9,8},{10,11... | collective-permute-start | bytes 3538952 | tf_op jit(solution)/shard_map/ppermute | solution.py:183
  150.6 2.9 %collective-permute-start.5 = (bf16[16,9,32,128]{3,2,1,0:T(8,128)(2,1)S(1)}, bf16[16,9,32,128]{3,2,1,0:T(8,128)(2,1)S(1)}, u32[]{:S(2)}, u32[]{:S(2)}) collective-permute-start(bf16[16,9,32,128]{3,2,1,0:T(8,128)(2,1)S(1)} %get-tuple-element.13), channel_id=1, source_target_pairs={{0,1},{1,0},{2,3},{3,2},{4,5},{5,4},{6,7},{7,6},{8,9},{9,8},{10,11... | collective-permute-start | bytes 3538952 | tf_op jit(solution)/shard_map/ppermute | solution.py:183
  153.8 38.8 %copy-start.1 = (bf16[8,3,256,256]{3,2,1,0:T(8,128)(2,1)S(1)}, bf16[8,3,256,256]{3,2,1,0:T(8,128)(2,1)}, u32[]{:S(2)}) copy-start(bf16[8,3,256,256]{3,2,1,0:T(8,128)(2,1)} %near_ref.3) | copy-start | bytes 9437188
  174.7 20.2 %all-to-all-start.7 = ((bf16[4,9,32,128]{3,2,1,0:T(8,128)(2,1)}), bf16[4,9,32,128]{3,2,1,0:T(8,128)(2,1)}, u32[]{:S(2)}, u32[]{:S(2)}) async-start(bf16[4,9,32,128]{3,2,1,0:T(8,128)(2,1)} %reduce_sum.25), calls=%async_computation.7 | async-start | bytes 589824 | tf_op jit(solution)/shard_map/all_to_all | solution.py:178
  179.5 8.1 %collective-permute-start.6 = (bf16[1,32,256]{2,1,0:T(8,128)(2,1)S(1)}, bf16[1,32,256]{2,1,0:T(8,128)(2,1)S(1)}, u32[]{:S(2)}, u32[]{:S(2)}) collective-permute-start(bf16[1,32,256]{2,1,0:T(8,128)(2,1)S(1)} %get-tuple-element.15), channel_id=1, source_target_pairs={{0,1},{1,2},{2,3},{3,4},{4,5},{5,6},{6,7},{7,8},{8,9},{9,10},{10,1... | collective-permute-start | bytes 49160 | tf_op jit(solution)/shard_map/ppermute | solution.py:252
  185.7 6.9 %collective-permute-start.7 = (bf16[1,32,256]{2,1,0:T(8,128)(2,1)S(1)}, bf16[1,32,256]{2,1,0:T(8,128)(2,1)S(1)}, u32[]{:S(2)}, u32[]{:S(2)}) collective-permute-start(bf16[1,32,256]{2,1,0:T(8,128)(2,1)S(1)} %get-tuple-element.14), channel_id=1, source_target_pairs={{1,0},{2,1},{3,2},{4,3},{5,4},{6,5},{7,6},{8,7},{9,8},{10,9},{11,1... | collective-permute-start | bytes 49160 | tf_op jit(solution)/shard_map/ppermute | solution.py:253
  192.6 0.9 copy-start.13
  194.1 0.7 copy-start.9
  194.8 0.9 copy-start.6
  195.7 0.9 copy-start.10

commit v3 on v2

v3 whole, which is shorter than its diff:
```python
import functools

import jax
import jax.numpy as jnp
from jax import lax
from jax.experimental import pallas as pl
from jax.experimental.pallas import tpu as pltpu
from jax.sharding import PartitionSpec as P

LANES = 128
BF = jnp.bfloat16
F32 = jnp.float32
VMEM = pl.BlockSpec(memory_space=pltpu.VMEM)
SMEM = pl.BlockSpec(memory_space=pltpu.SMEM)
HBM = pl.BlockSpec(memory_space=pltpu.HBM)


def dot(a, b):
    return lax.dot_general(a, b, (((1,), (0,)), ((), ())), preferred_element_type=F32)


def dot_t(a, b):
    return lax.dot_general(a, b, (((1,), (1,)), ((), ())), preferred_element_type=F32)


def lanes(rows):
    return lax.broadcasted_iota(jnp.int32, (rows, LANES), 1)


def fourth(tiles, rank_top):
    third = LANES - rank_top
    lane = lanes(tiles[0].shape[0])
    moved = [pltpu.roll(tile, third * (k + 1), 1) for k, tile in enumerate(tiles)]
    return jnp.where(lane < third, moved[0], jnp.where(lane < 2 * third, moved[1], moved[2]))


def packed(mains, pad, rank_top):
    lane = lanes(pad.shape[0])
    third = LANES - rank_top
    return [
        jnp.where(lane < rank_top, main, pltpu.roll(pad, rank_top - third * k, 1)) for k, main in enumerate(mains)
    ]


def widen(value):
    return jnp.concatenate([value, jnp.zeros((value.shape[0], LANES - value.shape[1]), value.dtype)], axis=1)


def emit_coeffs(read_leaf, basis_ref, transfer_ref, ranks_ref, out_ref, leaves, rank_top):
    mains, rhs, _ = out_ref.shape
    lane = lax.broadcasted_iota(jnp.int32, (rhs, rank_top), 1)
    coeffs = []
    for i in range(leaves):
        value = dot_t(read_leaf(i), basis_ref[i])
        coeffs.append(jnp.where(lane < ranks_ref[i], value, 0.0).astype(BF))
    for q in range(leaves // 2):
        value = dot(coeffs[2 * q], transfer_ref[2 * q]) + dot(coeffs[2 * q + 1], transfer_ref[2 * q + 1])
        coeffs.append(jnp.where(lane < ranks_ref[leaves + q], value, 0.0).astype(BF))
    wide = [widen(value.astype(F32)) for value in coeffs]
    for q in range(mains // 3):
        for k, tile in enumerate(packed(wide[3 * q : 3 * q + 3], wide[mains + q], rank_top)):
            out_ref[3 * q + k] = tile.astype(BF)


def fetch(pairs, sems):
    copies = [pltpu.make_async_copy(src, dst, sems.at[n]) for n, (src, dst) in enumerate(pairs)]
    for copy in copies:
        copy.start()
    return copies


def coeff_kernel(ranks_ref, v_hbm, basis_hbm, transfer_hbm, out_ref, v_ref, basis_ref, transfer_ref, sems):
    leaves, rank_top, _ = basis_ref.shape
    for copy in fetch([(v_hbm, v_ref), (basis_hbm, basis_ref), (transfer_hbm, transfer_ref)], sems):
        copy.wait()
    emit_coeffs(lambda i: v_ref[i], basis_ref, transfer_ref, ranks_ref, out_ref, leaves, rank_top)


def couple_kernel(source_ref, target_ref, own_ref, other_ref, coupling_ref, keep_ref, send_ref, sources, total, *, unroll):
    blocks, rank_top, _ = coupling_ref.shape
    devices, mains, rhs, _ = own_ref.shape
    quads = mains // 3
    clusters = mains + quads

    def split(d, _):
        for half, packed_ref in enumerate((own_ref, other_ref)):
            row = (half * devices + d) * clusters
            tiles = [packed_ref[d, c] for c in range(mains)]
            for c in range(mains):
                sources[row + c] = tiles[c]
            for q in range(quads):
                wide = [tile.astype(F32) for tile in tiles[3 * q : 3 * q + 3]]
                sources[row + mains + q] = fourth(wide, rank_top).astype(BF)
            for c in range(clusters):
                total[row + c] = jnp.zeros((rhs, LANES), F32)
        return 0

    lax.fori_loop(0, devices, split, 0, unroll=2)

    def some(s, _):
        for u in range(unroll):
            j = s * unroll + u
            term = dot(sources[source_ref[j], :, :rank_top], coupling_ref[j])
            at = target_ref[j]
            total[at, :, :rank_top] = total[at, :, :rank_top] + term
        return 0

    lax.fori_loop(0, blocks // unroll, some, 0)

    def pack(d, _):
        for half, packed_ref in enumerate((keep_ref, send_ref)):
            row = (half * devices + d) * clusters
            for q in range(quads):
                mains_now = [total[row + 3 * q + k] for k in range(3)]
                for k, tile in enumerate(packed(mains_now, total[row + mains + q], rank_top)):
                    packed_ref[d, 3 * q + k] = tile.astype(BF)
        return 0

    lax.fori_loop(0, devices, pack, 0, unroll=2)


def near_kernel(v_ref, before_ref, after_ref, near_ref, out_ref):
    leaves = v_ref.shape[0]
    for i in range(leaves):
        left = v_ref[i - 1] if i > 0 else before_ref[0]
        right = v_ref[i + 1] if i < leaves - 1 else after_ref[0]
        out_ref[i] = dot(left, near_ref[i, 0]) + dot(v_ref[i], near_ref[i, 1]) + dot(right, near_ref[i, 2])


def sum_kernel(parts_ref, keep_ref, send_ref):
    parts, far, mains, _, _ = parts_ref.shape
    for f in range(far):
        for t in range(mains):
            tile = parts_ref[0, f, t].astype(F32)
            for p in range(1, parts):
                tile = tile + parts_ref[p, f, t].astype(F32)
            if f == 0:
                keep_ref[t] = tile
            else:
                send_ref[f - 1, t] = tile.astype(BF)


def field_kernel(ranks_ref, keep_ref, terms_ref, near_hbm, basis_hbm, transfer_hbm, out_ref, *rest):
    *coeff_ref, near_ref, basis_ref, transfer_ref, sems = rest
    copies = fetch([(transfer_hbm, transfer_ref), (basis_hbm, basis_ref), (near_hbm, near_ref)], sems)
    leaves, rank_top, _ = basis_ref.shape
    parts, mains, rhs, _ = terms_ref.shape
    tiles = []
    for t in range(mains):
        tile = keep_ref[t]
        for p in range(parts):
            tile = tile + terms_ref[p, t].astype(F32)
        tiles.append(tile)
    sums = tiles + [fourth(tiles[3 * q : 3 * q + 3], rank_top) for q in range(mains // 3)]
    lane = lax.broadcasted_iota(jnp.int32, (rhs, rank_top), 1)
    fields = [
        jnp.where(lane < ranks_ref[c], total[:, :rank_top], 0.0).astype(BF) for c, total in enumerate(sums)
    ]
    for copy in copies:
        copy.wait()
    for i in range(leaves):
        down = fields[i].astype(F32) + dot_t(fields[leaves + i // 2], transfer_ref[i])
        leaf_total = jnp.where(lane < ranks_ref[i], down, 0.0).astype(BF)
        out_ref[i] = (near_ref[i] + dot(leaf_total, basis_ref[i])).astype(BF)
    if coeff_ref:
        emit_coeffs(lambda i: out_ref[i], basis_ref, transfer_ref, ranks_ref, coeff_ref[0], leaves, rank_top)


def params(mebibytes):
    return pltpu.CompilerParams(vmem_limit_bytes=mebibytes << 20)


def local(charges, basis, transfer, near_field, coupling, ranks, block_source, block_target):
    leaves, rank_top, width = basis.shape
    rhs = charges.shape[1]
    clusters = ranks.shape[0]
    blocks = coupling.shape[0]
    devices = lax.axis_size("clu")
    mains = clusters * 3 // 4
    shape = jax.ShapeDtypeStruct

    cores, chips = 2, 8
    cube = cores * chips
    far = devices // cube
    half = chips * far
    cube_groups = [[f * cube + q * cores + k for q in range(chips)] for f in range(far) for k in range(cores)]

    def exchange(parts):
        return lax.all_to_all(
            parts, "clu", split_axis=0, concat_axis=0, tiled=True, axis_index_groups=cube_groups
        )

    def swap_far(part, shift):
        return lax.ppermute(part, "clu", [(d, (d + shift * cube) % devices) for d in range(devices)])

    def swap_cores(part):
        return lax.ppermute(part, "clu", [(d, d ^ 1) for d in range(devices)])

    me = lax.axis_index("clu")

    def rows(cluster, sign):
        device = cluster // clusters
        core = (device + me) % cores
        chip = (device // cores) % chips
        away = (sign * (device // cube - me // cube)) % far
        return ((core * chips + chip) * far + away) * clusters + cluster % clusters

    source_rows, target_rows = rows(block_source, -1), rows(block_target, 1)

    tile_shape = (mains, rhs, LANES)
    out_shape = shape((leaves, rhs, width), BF)
    half_shape = shape((half,) + tile_shape, BF)
    weights = [pltpu.VMEM(basis.shape, BF), pltpu.VMEM(transfer.shape, BF), pltpu.SemaphoreType.DMA((3,))]
    first_coeffs = pl.pallas_call(
        coeff_kernel,
        out_shape=shape(tile_shape, BF),
        in_specs=[SMEM, HBM, HBM, HBM],
        out_specs=VMEM,
        scratch_shapes=[pltpu.VMEM(charges.shape, BF)] + weights,
        compiler_params=params(16),
    )(ranks, charges, basis, transfer)

    couple = pl.pallas_call(
        functools.partial(couple_kernel, unroll=8),
        out_shape=[half_shape, half_shape],
        in_specs=[SMEM, SMEM, VMEM, VMEM, VMEM],
        out_specs=[VMEM, VMEM],
        scratch_shapes=[
            pltpu.VMEM((devices * clusters, rhs, LANES), BF),
            pltpu.VMEM((devices * clusters, rhs, LANES), F32),
        ],
        compiler_params=params(32 if devices <= 32 else 60),
        cost_estimate=pl.CostEstimate(
            flops=2 * blocks * rhs * rank_top * rank_top, bytes_accessed=10 << 20, transcendentals=0
        ),
    )

    near = pl.pallas_call(
        near_kernel,
        out_shape=shape((leaves, rhs, width), F32),
        in_specs=[VMEM] * 4,
        out_specs=VMEM,
        compiler_params=params(16),
        cost_estimate=pl.CostEstimate(
            flops=2 * leaves * 3 * rhs * width * width, bytes_accessed=4 << 20, transcendentals=0
        ),
    )

    add_parts = pl.pallas_call(
        sum_kernel,
        out_shape=[shape(tile_shape, F32), shape((far - 1,) + tile_shape, BF)],
        in_specs=[VMEM],
        out_specs=[VMEM, VMEM],
        compiler_params=params(16),
    )

    def finish(with_coeffs):
        return pl.pallas_call(
            field_kernel,
            out_shape=[out_shape, shape(tile_shape, BF)] if with_coeffs else [out_shape],
            in_specs=[SMEM, VMEM, VMEM, HBM, HBM, HBM],
            out_specs=[VMEM, VMEM] if with_coeffs else [VMEM],
            scratch_shapes=[pltpu.VMEM((leaves, rhs, width), F32)] + weights,
            compiler_params=params(16),
        )

    ends = devices - 1

    def apply_matrix(field_in, coeffs, with_coeffs):
        column = jnp.stack([coeffs] + [swap_far(coeffs, s) for s in range(1, far)])
        own = exchange(jnp.broadcast_to(column[None], (chips,) + column.shape))
        before = lax.ppermute(field_in[leaves - 1 :], "clu", [(i, i + 1) for i in range(ends)])
        after = lax.ppermute(field_in[:1], "clu", [(i + 1, i) for i in range(ends)])
        near_sum = near(field_in, before, after, near_field)
        own, near_sum = lax.optimization_barrier((own, near_sum))
        own = own.reshape(half_shape.shape)
        other = swap_cores(own)
        keep, send = couple(source_rows, target_rows, own, other, coupling)
        chip_sum = keep.astype(F32) + swap_cores(send).astype(F32)
        parts = exchange(chip_sum.astype(BF).reshape((chips, far) + tile_shape))
        mine, away = add_parts(parts)
        terms = jnp.concatenate([swap_far(away[s - 1 : s], s) for s in range(1, far)])
        return finish(with_coeffs)(ranks, mine, terms, near_sum, basis, transfer)

    first, second_coeffs = apply_matrix(charges, first_coeffs, True)
    (second,) = apply_matrix(first, second_coeffs, False)
    return (first, second)


def solution(mesh):
    in_specs = (
        P("clu", None, None),
        P("clu", None, None),
        P("clu", None, None),
        P("clu", None, None, None),
        P("clu", None, None),
        P("clu"),
        P("clu"),
        P("clu"),
    )
    out_specs = (P("clu", None, None), P("clu", None, None))
    return jax.shard_map(local, mesh=mesh, in_specs=in_specs, out_specs=out_specs, check_vma=False)
```

time: 201 us -> 153 us (0.76)
  the two profiles are of different devices: /device:TPU:7 before, /device:TPU:0 now
where the time goes in v3:
time: 153 us
  blocking collectives  41.3 us (27%)
  waiting for transfers between devices  38 us (25%)
  starting transfers between devices  33.5 us (22%)
  Pallas kernels  23.6 us (15%)
  local copies, waits for them, and re-layouts  14.5 us (9%)
    all_to_all x2, blocking collectives, exchange(): lax.all_to_all(parts, 'clu', split_axis=0, concat_axis=0, tiled=True, axi...  41.3 us
    ppermute x4, waiting for transfers between devices, swap_far(): lax.ppermute(part, 'clu', [(d, (d + shift * cube) % devices) for d in ran...  14.9 us
    pallas_call x2, Pallas kernels, apply_matrix(): keep, send = couple(source_rows, target_rows, own, other, coupling)  14.3 us
    all_to_all x2, waiting for transfers between devices, exchange(): lax.all_to_all(parts, 'clu', split_axis=0, concat_axis=0, tiled=True, axi...  13.4 us
    ppermute x4, starting transfers between devices, swap_far(): lax.ppermute(part, 'clu', [(d, (d + shift * cube) % devices) for d in ran...  11.3 us
    unnamed x37, local copies, waits for them, and re-layouts  11.3 us
    all_to_all x2, starting transfers between devices, exchange(): lax.all_to_all(parts, 'clu', split_axis=0, concat_axis=0, tiled=True, axi...  8.63 us
    ppermute x4, waiting for transfers between devices, swap_cores(): return lax.ppermute(part, 'clu', [(d, d ^ 1) for d in range(devices)])  8 us
  transfers between devices with their start and end apart: 14, of which 11 were waited for; matrix products, arithmetic and copies ran while one was open for 3% of the time, Pallas kernels for 1%

profile of v3, /device:TPU:0, one launch (start us, length us, event | category | flops | bytes accessed | tf_op | source)
XLA Modules:
  0.0 152.5 jit_solution(6115064028084657667)
XLA Ops:
  0.6 0.0 copy-start.2
  0.6 1.0 copy-done.2
  1.6 0.9 copy-done.4
  2.6 0.9 copy-done.11
  3.5 0.7 copy-done.14
  4.1 1.6 %shard_map.95 = bf16[9,32,128]{2,1,0:T(8,128)(2,1)S(1)} custom-call(s32[12]{0:T(128)S(1)} %copy-done.14, bf16[8,32,256]{2,1,0:T(8,128)(2,1)S(1)} %copy-done.11, bf16[8,96,256]{2,1,0:T(8,128)(2,1)S(1)} %copy-done.2, bf16[8,96,96]{2,1,0:T(8,128)(2,1)S(1)} %copy-done.4), custom_call_target="tpu_custom_call" | custom-call | tf_op jit(solution)/shard_map/pallas_call | solution.py:214
  5.8 4.1 %collective-permute-start = (bf16[9,32,128]{2,1,0:T(8,128)(2,1)S(1)}, bf16[9,32,128]{2,1,0:T(8,128)(2,1)S(1)}, u32[]{:S(2)}, u32[]{:S(2)}) collective-permute-start(bf16[9,32,128]{2,1,0:T(8,128)(2,1)S(1)} %shard_map.95), channel_id=1, source_target_pairs={{0,16},{1,17},{2,18},{3,19},{4,20},{5,21},{6,22},{7,23},{8,24},{9,... | collective-permute-start | bytes 221192 | tf_op jit(solution)/shard_map/ppermute | solution.py:194
  9.9 3.9 %collective-permute-done = bf16[9,32,128]{2,1,0:T(8,128)(2,1)S(1)} collective-permute-done((bf16[9,32,128]{2,1,0:T(8,128)(2,1)S(1)}, bf16[9,32,128]{2,1,0:T(8,128)(2,1)S(1)}, u32[]{:S(2)}, u32[]{:S(2)}) %collective-permute-start) | collective-permute-done | bytes 73760 | tf_op jit(solution)/shard_map/ppermute | solution.py:194
  13.8 0.0 copy-start
  13.8 1.2 broadcast_in_dim.4
  15.0 4.4 %all-to-all-start = ((bf16[8,2,9,32,128]{4,3,2,1,0:T(8,128)(2,1)}), bf16[8,2,9,32,128]{4,3,2,1,0:T(8,128)(2,1)}, u32[]{:S(2)}, u32[]{:S(2)}) async-start(bf16[8,2,9,32,128]{4,3,2,1,0:T(8,128)(2,1)} %broadcast_in_dim.4), calls=%async_computation | async-start | bytes 2359296 | tf_op jit(solution)/shard_map/all_to_all | solution.py:189
  19.4 0.0 copy-done.12
  19.5 1.3 collective-permute-start.2
  20.8 3.0 %collective-permute-start.1 = (bf16[1,32,256]{2,1,0:T(8,128)(2,1)S(1)}, bf16[1,32,256]{2,1,0:T(8,128)(2,1)S(1)}, u32[]{:S(2)}, u32[]{:S(2)}) collective-permute-start(bf16[1,32,256]{2,1,0:T(8,128)(2,1)S(1)} %get-tuple-element.33), channel_id=1, source_target_pairs={{0,1},{1,2},{2,3},{3,4},{4,5},{5,6},{6,7},{7,8},{8,9},{9,10},{10,1... | collective-permute-start | bytes 49160 | tf_op jit(solution)/shard_map/ppermute | solution.py:272
  23.8 0.0 collective-permute-done.2.after_ref
  23.8 0.8 collective-permute-done.1.before_ref
  24.6 0.0 copy-done
  24.6 0.6 shard_map.96.near_hbm
  25.2 0.7 copy-done.7
  26.0 9.2 %all-to-all-done = bf16[8,2,9,32,128]{4,3,2,1,0:T(8,128)(2,1)} async-done(((bf16[8,2,9,32,128]{4,3,2,1,0:T(8,128)(2,1)}), bf16[8,2,9,32,128]{4,3,2,1,0:T(8,128)(2,1)}, u32[]{:S(2)}, u32[]{:S(2)}) %all-to-all-start) | async-done | bytes 1179680 | tf_op jit(solution)/shard_map/all_to_all | solution.py:189
  35.2 0.9 collective-permute-start.3
  36.1 3.6 %copy.10.coupling_ref = bf16[128,96,96]{2,1,0:T(8,128)(2,1)S(1)} copy(bf16[128,96,96]{0,2,1:T(8,128)(2,1)} %param.12) | data formatting | bytes 4718592 | tf_op args[4]
  39.7 0.0 copy-done.16
  39.7 0.0 copy-done.17
  39.7 0.0 collective-permute-done.3.other_ref
  39.7 7.3 %shard_map.97 = (bf16[16,9,32,128]{3,2,1,0:T(8,128)(2,1)S(1)}, bf16[16,9,32,128]{3,2,1,0:T(8,128)(2,1)S(1)}) custom-call(s32[128]{0:T(128)S(1)} %get-tuple-element.34.source_ref, s32[128]{0:T(128)S(1)} %get-tuple-element.35.target_ref, bf16[16,9,32,128]{3,2,1,0:T(8,128)(2,1)} %bitcast.2.own_ref, bf16[16,9,32,128]{3,2,1,0:T(8,128)(2,1)} %collective-permute-done.3.other_ref, ...), custom_call_target="tpu_custom_call" | custom-call | flops 75497472 | bytes 10485760 | tf_op jit(solution)/shard_map/pallas_call | solution.py:278
  47.1 0.1 collective-permute-start.4
  47.2 2.8 %collective-permute-done.4 = bf16[16,9,32,128]{3,2,1,0:T(8,128)(2,1)S(1)} collective-permute-done((bf16[16,9,32,128]{3,2,1,0:T(8,128)(2,1)S(1)}, bf16[16,9,32,128]{3,2,1,0:T(8,128)(2,1)S(1)}, u32[]{:S(2)}, u32[]{:S(2)}) %collective-permute-start.4) | collective-permute-done | bytes 1179680 | tf_op jit(solution)/shard_map/ppermute | solution.py:197
  50.0 0.3 add_convert_fusion.1
  50.3 20.9 %all_to_all.20.parts_ref = bf16[8,2,9,32,128]{4,3,2,1,0:T(8,128)(2,1)S(1)} all-to-all(bf16[8,2,9,32,128]{4,3,2,1,0:T(8,128)(2,1)S(1)} %bitcast.10), channel_id=1, replica_groups={{0,2,4,6,8,10,12,14},{1,3,5,7,9,11,13,15},{16,18,20,22,24,26,28,30},{17..., dimensions={0} | all-to-all | bytes 2359296 | tf_op jit(solution)/shard_map/all_to_all | solution.py:189
  71.3 0.2 shard_map.98
  71.4 3.5 %collective-permute-start.5 = (bf16[1,9,32,128]{3,2,1,0:T(8,128)(2,1)S(1)}, bf16[1,9,32,128]{3,2,1,0:T(8,128)(2,1)S(1)}, u32[]{:S(2)}, u32[]{:S(2)}) collective-permute-start(bf16[1,9,32,128]{3,2,1,0:T(8,128)(2,1)S(1)} %get-tuple-element.20), channel_id=1, source_target_pairs={{0,16},{1,17},{2,18},{3,19},{4,20},{5,21},{6,22},{7,23},{8,24},{9,... | collective-permute-start | bytes 221192 | tf_op jit(solution)/shard_map/ppermute | solution.py:194
  75.0 3.1 %collective-permute-done.5.terms_ref = bf16[1,9,32,128]{3,2,1,0:T(8,128)(2,1)S(1)} collective-permute-done((bf16[1,9,32,128]{3,2,1,0:T(8,128)(2,1)S(1)}, bf16[1,9,32,128]{3,2,1,0:T(8,128)(2,1)S(1)}, u32[]{:S(2)}, u32[]{:S(2)}) %collective-permute-start.5) | collective-permute-done | bytes 73760 | tf_op jit(solution)/shard_map/ppermute | solution.py:194
  78.1 0.0 copy-done.3
  78.1 0.0 copy-done.5
  78.1 0.0 copy-done.8
  78.1 0.0 copy-done.15
  78.1 3.0 %shard_map.99 = (bf16[8,32,256]{2,1,0:T(8,128)(2,1)}, bf16[9,32,128]{2,1,0:T(8,128)(2,1)S(1)}) custom-call(s32[12]{0:T(128)S(1)} %copy-done.15, f32[9,32,128]{2,1,0:T(8,128)S(1)} %get-tuple-element.19.keep_ref, bf16[1,9,32,128]{3,2,1,0:T(8,128)(2,1)S(1)} %collective-permute-done.5.terms_ref, f32[8,32,256]{2,1,0:T(8,128)S(1)} %copy-done.8, ...), custom_call_target="tpu_custom_call" | custom-call | tf_op jit(solution)/shard_map/pallas_call | solution.py:283
  81.2 2.3 %collective-permute-start.6 = (bf16[9,32,128]{2,1,0:T(8,128)(2,1)S(1)}, bf16[9,32,128]{2,1,0:T(8,128)(2,1)S(1)}, u32[]{:S(2)}, u32[]{:S(2)}) collective-permute-start(bf16[9,32,128]{2,1,0:T(8,128)(2,1)S(1)} %get-tuple-element.23), channel_id=1, source_target_pairs={{0,16},{1,17},{2,18},{3,19},{4,20},{5,21},{6,22},{7,23},{8,24},{9,... | collective-permute-start | bytes 221192 | tf_op jit(solution)/shard_map/ppermute | solution.py:194
  83.4 3.2 %collective-permute-done.6 = bf16[9,32,128]{2,1,0:T(8,128)(2,1)S(1)} collective-permute-done((bf16[9,32,128]{2,1,0:T(8,128)(2,1)S(1)}, bf16[9,32,128]{2,1,0:T(8,128)(2,1)S(1)}, u32[]{:S(2)}, u32[]{:S(2)}) %collective-permute-start.6) | collective-permute-done | bytes 73760 | tf_op jit(solution)/shard_map/ppermute | solution.py:194
  86.7 1.2 broadcast_in_dim.5
  87.9 4.2 %all-to-all-start.2 = ((bf16[8,2,9,32,128]{4,3,2,1,0:T(8,128)(2,1)}), bf16[8,2,9,32,128]{4,3,2,1,0:T(8,128)(2,1)}, u32[]{:S(2)}, u32[]{:S(2)}) async-start(bf16[8,2,9,32,128]{4,3,2,1,0:T(8,128)(2,1)} %broadcast_in_dim.5), calls=%async_computation.2 | async-start | bytes 2359296 | tf_op jit(solution)/shard_map/all_to_all | solution.py:189
  92.2 0.7 fusion.14
  92.9 1.3 collective-permute-start.8
  94.2 3.0 %collective-permute-start.7 = (bf16[1,32,256]{2,1,0:T(8,128)(2,1)S(1)}, bf16[1,32,256]{2,1,0:T(8,128)(2,1)S(1)}, u32[]{:S(2)}, u32[]{:S(2)}) collective-permute-start(bf16[1,32,256]{2,1,0:T(8,128)(2,1)S(1)} %get-tuple-element.31), channel_id=1, source_target_pairs={{0,1},{1,2},{2,3},{3,4},{4,5},{5,6},{6,7},{7,8},{8,9},{9,10},{10,1... | collective-permute-start | bytes 49160 | tf_op jit(solution)/shard_map/ppermute | solution.py:272
  97.2 0.0 collective-permute-done.8.after_ref
  97.3 0.8 collective-permute-done.7.before_ref
  98.1 1.9 %copy-done.1 = bf16[8,3,256,256]{3,2,1,0:T(8,128)(2,1)S(1)} copy-done((bf16[8,3,256,256]{3,2,1,0:T(8,128)(2,1)S(1)}, bf16[8,3,256,256]{3,2,1,0:T(8,128)(2,1)}, u32[]{:S(2)}) %copy-start.1) | copy-done | bytes 3145752
  100.0 0.9 copy-done.13
  100.9 0.6 shard_map.100.near_hbm
  101.5 0.7 copy-done.9
  102.2 4.2 %all-to-all-done.2 = bf16[8,2,9,32,128]{4,3,2,1,0:T(8,128)(2,1)} async-done(((bf16[8,2,9,32,128]{4,3,2,1,0:T(8,128)(2,1)}), bf16[8,2,9,32,128]{4,3,2,1,0:T(8,128)(2,1)}, u32[]{:S(2)}, u32[]{:S(2)}) %all-to-all-start.2) | async-done | bytes 1179680 | tf_op jit(solution)/shard_map/all_to_all | solution.py:189
  106.4 3.5 %collective-permute-start.9 = (bf16[16,9,32,128]{3,2,1,0:T(8,128)(2,1)}, bf16[16,9,32,128]{3,2,1,0:T(8,128)(2,1)S(1)}, u32[]{:S(2)}, u32[]{:S(2)}) collective-permute-start(bf16[16,9,32,128]{3,2,1,0:T(8,128)(2,1)} %bitcast.6.own_ref), channel_id=1, source_target_pairs={{0,1},{1,0},{2,3},{3,2},{4,5},{5,4},{6,7},{7,6},{8,9},{9,8},{10,11... | collective-permute-start | bytes 3538952 | tf_op jit(solution)/shard_map/ppermute | solution.py:197
  109.9 2.7 %collective-permute-done.9.other_ref = bf16[16,9,32,128]{3,2,1,0:T(8,128)(2,1)S(1)} collective-permute-done((bf16[16,9,32,128]{3,2,1,0:T(8,128)(2,1)}, bf16[16,9,32,128]{3,2,1,0:T(8,128)(2,1)S(1)}, u32[]{:S(2)}, u32[]{:S(2)}) %collective-permute-start.9) | collective-permute-done | bytes 1179680 | tf_op jit(solution)/shard_map/ppermute | solution.py:197
  112.6 7.0 %shard_map.101 = (bf16[16,9,32,128]{3,2,1,0:T(8,128)(2,1)S(1)}, bf16[16,9,32,128]{3,2,1,0:T(8,128)(2,1)S(1)}) custom-call(s32[128]{0:T(128)S(1)} %get-tuple-element.34.source_ref, s32[128]{0:T(128)S(1)} %get-tuple-element.35.target_ref, bf16[16,9,32,128]{3,2,1,0:T(8,128)(2,1)} %bitcast.6.own_ref, ...), custom_call_target="tpu_custom_call" | custom-call | flops 75497472 | bytes 10485760 | tf_op jit(solution)/shard_map/pallas_call | solution.py:278
  119.6 0.4 collective-permute-start.10
  120.1 2.5 %collective-permute-done.10 = bf16[16,9,32,128]{3,2,1,0:T(8,128)(2,1)S(1)} collective-permute-done((bf16[16,9,32,128]{3,2,1,0:T(8,128)(2,1)S(1)}, bf16[16,9,32,128]{3,2,1,0:T(8,128)(2,1)S(1)}, u32[]{:S(2)}, u32[]{:S(2)}) %collective-permute-start.10) | collective-permute-done | bytes 1179680 | tf_op jit(solution)/shard_map/ppermute | solution.py:197
  122.5 0.3 add_convert_fusion
  122.8 20.4 %all_to_all.21.parts_ref = bf16[8,2,9,32,128]{4,3,2,1,0:T(8,128)(2,1)S(1)} all-to-all(bf16[8,2,9,32,128]{4,3,2,1,0:T(8,128)(2,1)S(1)} %bitcast.11), channel_id=1, replica_groups={{0,2,4,6,8,10,12,14},{1,3,5,7,9,11,13,15},{16,18,20,22,24,26,28,30},{17..., dimensions={0} | all-to-all | bytes 2359296 | tf_op jit(solution)/shard_map/all_to_all | solution.py:189
  143.2 0.2 shard_map.102
  143.4 1.4 collective-permute-start.11
  144.8 4.7 %collective-permute-done.11.terms_ref = bf16[1,9,32,128]{3,2,1,0:T(8,128)(2,1)S(1)} collective-permute-done((bf16[1,9,32,128]{3,2,1,0:T(8,128)(2,1)S(1)}, bf16[1,9,32,128]{3,2,1,0:T(8,128)(2,1)S(1)}, u32[]{:S(2)}, u32[]{:S(2)}) %collective-permute-start.11) | collective-permute-done | bytes 73760 | tf_op jit(solution)/shard_map/ppermute | solution.py:194
  149.5 0.0 copy-done.10
  149.5 3.0 %shard_map.103 = bf16[8,32,256]{2,1,0:T(8,128)(2,1)} custom-call(s32[12]{0:T(128)S(1)} %copy-done.15, f32[9,32,128]{2,1,0:T(8,128)S(1)} %get-tuple-element.27.keep_ref, bf16[1,9,32,128]{3,2,1,0:T(8,128)(2,1)S(1)} %collective-permute-done.11.terms_ref, f32[8,32,256]{2,1,0:T(8,128)S(1)} %copy-done.10, bf16[8,96,256]{2,1,0:T(8,128)(2,1)S(1)} %copy-done.3, ...), custom_call_target="tpu_custom_call" | custom-call | tf_op jit(solution)/shard_map/pallas_call | solution.py:283
  (21 shorter events, 0.1 us)
Async XLA Ops:
  0.6 1.0 copy-start.2
  1.6 0.9 copy-start.4
  2.6 0.9 copy-start.11
  3.5 0.7 copy-start.14
  5.8 8.0 %collective-permute-start = (bf16[9,32,128]{2,1,0:T(8,128)(2,1)S(1)}, bf16[9,32,128]{2,1,0:T(8,128)(2,1)S(1)}, u32[]{:S(2)}, u32[]{:S(2)}) collective-permute-start(bf16[9,32,128]{2,1,0:T(8,128)(2,1)S(1)} %shard_map.95), channel_id=1, source_target_pairs={{0,16},{1,17},{2,18},{3,19},{4,20},{5,21},{6,22},{7,23},{8,24},{9,... | collective-permute-start | bytes 221192 | tf_op jit(solution)/shard_map/ppermute | solution.py:194
  13.8 10.8 %copy-start = (bf16[8,3,256,256]{3,2,1,0:T(8,128)(2,1)S(1)}, bf16[8,3,256,256]{3,2,1,0:T(8,128)(2,1)}, u32[]{:S(2)}) copy-start(bf16[8,3,256,256]{3,2,1,0:T(8,128)(2,1)} %near_ref.3) | copy-start | bytes 9437188
  15.0 4.4 %copy-start.12 = (bf16[8,32,256]{2,1,0:T(8,128)(2,1)S(1)}, bf16[8,32,256]{2,1,0:T(8,128)(2,1)}, u32[]{:S(2)}) copy-start(bf16[8,32,256]{2,1,0:T(8,128)(2,1)} %v_ref.1) | copy-start | bytes 393220
  15.0 20.2 %all-to-all-start = ((bf16[8,2,9,32,128]{4,3,2,1,0:T(8,128)(2,1)}), bf16[8,2,9,32,128]{4,3,2,1,0:T(8,128)(2,1)}, u32[]{:S(2)}, u32[]{:S(2)}) async-start(bf16[8,2,9,32,128]{4,3,2,1,0:T(8,128)(2,1)} %broadcast_in_dim.4), calls=%async_computation | async-start | bytes 2359296 | tf_op jit(solution)/shard_map/all_to_all | solution.py:189
  19.5 4.3 %collective-permute-start.2 = (bf16[1,32,256]{2,1,0:T(8,128)(2,1)S(1)}, bf16[1,32,256]{2,1,0:T(8,128)(2,1)S(1)}, u32[]{:S(2)}, u32[]{:S(2)}) collective-permute-start(bf16[1,32,256]{2,1,0:T(8,128)(2,1)S(1)} %get-tuple-element.32), channel_id=1, source_target_pairs={{1,0},{2,1},{3,2},{4,3},{5,4},{6,5},{7,6},{8,7},{9,8},{10,9},{11,1... | collective-permute-start | bytes 49160 | tf_op jit(solution)/shard_map/ppermute | solution.py:273
  20.8 3.9 %collective-permute-start.1 = (bf16[1,32,256]{2,1,0:T(8,128)(2,1)S(1)}, bf16[1,32,256]{2,1,0:T(8,128)(2,1)S(1)}, u32[]{:S(2)}, u32[]{:S(2)}) collective-permute-start(bf16[1,32,256]{2,1,0:T(8,128)(2,1)S(1)} %get-tuple-element.33), channel_id=1, source_target_pairs={{0,1},{1,2},{2,3},{3,4},{4,5},{5,6},{6,7},{7,8},{8,9},{9,10},{10,1... | collective-permute-start | bytes 49160 | tf_op jit(solution)/shard_map/ppermute | solution.py:272
  25.2 0.7 copy-start.7
  35.2 4.5 %collective-permute-start.3 = (bf16[16,9,32,128]{3,2,1,0:T(8,128)(2,1)}, bf16[16,9,32,128]{3,2,1,0:T(8,128)(2,1)}, u32[]{:S(2)}, u32[]{:S(2)}) collective-permute-start(bf16[16,9,32,128]{3,2,1,0:T(8,128)(2,1)} %bitcast.2.own_ref), channel_id=1, source_target_pairs={{0,1},{1,0},{2,3},{3,2},{4,5},{5,4},{6,7},{7,6},{8,9},{9,8},{10,11... | collective-permute-start | bytes 3538952 | tf_op jit(solution)/shard_map/ppermute | solution.py:197
  36.1 3.6 %copy-start.16 = (s32[128]{0:T(128)S(1)}, s32[128]{0:T(128)}, u32[]{:S(2)}) copy-start(s32[128]{0:T(128)} %param.14) | copy-start | bytes 1540
  36.1 3.6 %copy-start.17 = (s32[128]{0:T(128)S(1)}, s32[128]{0:T(128)}, u32[]{:S(2)}) copy-start(s32[128]{0:T(128)} %param.15) | copy-start | bytes 1540
  47.1 2.9 %collective-permute-start.4 = (bf16[16,9,32,128]{3,2,1,0:T(8,128)(2,1)S(1)}, bf16[16,9,32,128]{3,2,1,0:T(8,128)(2,1)S(1)}, u32[]{:S(2)}, u32[]{:S(2)}) collective-permute-start(bf16[16,9,32,128]{3,2,1,0:T(8,128)(2,1)S(1)} %get-tuple-element.18), channel_id=1, source_target_pairs={{0,1},{1,0},{2,3},{3,2},{4,5},{5,4},{6,7},{7,6},{8,9},{9,8},{10,11... | collective-permute-start | bytes 3538952 | tf_op jit(solution)/shard_map/ppermute | solution.py:197
  71.3 6.8 %copy-start.3 = (bf16[8,96,256]{2,1,0:T(8,128)(2,1)S(1)}, bf16[8,96,256]{2,1,0:T(8,128)(2,1)}, u32[]{:S(2)}) copy-start(bf16[8,96,256]{2,1,0:T(8,128)(2,1)} %basis_hbm.5) | copy-start | bytes 1179652
  71.3 6.8 %copy-start.5 = (bf16[8,96,96]{2,1,0:T(8,128)(2,1)S(1)}, bf16[8,96,96]{2,1,0:T(8,128)(2,1)}, u32[]{:S(2)}) copy-start(bf16[8,96,96]{2,1,0:T(8,128)(2,1)} %transfer_hbm.5) | copy-start | bytes 442372
  71.3 6.8 %copy-start.8 = (f32[8,32,256]{2,1,0:T(8,128)S(1)}, f32[8,32,256]{2,1,0:T(8,128)}, u32[]{:S(2)}) copy-start(f32[8,32,256]{2,1,0:T(8,128)} %copy-done.7) | copy-start | bytes 786436
  71.3 6.8 %copy-start.15 = (s32[12]{0:T(128)S(1)}, s32[12]{0:T(128)}, u32[]{:S(2)}) copy-start(s32[12]{0:T(128)} %ranks_ref.5) | copy-start | bytes 148
  71.4 6.6 %collective-permute-start.5 = (bf16[1,9,32,128]{3,2,1,0:T(8,128)(2,1)S(1)}, bf16[1,9,32,128]{3,2,1,0:T(8,128)(2,1)S(1)}, u32[]{:S(2)}, u32[]{:S(2)}) collective-permute-start(bf16[1,9,32,128]{3,2,1,0:T(8,128)(2,1)S(1)} %get-tuple-element.20), channel_id=1, source_target_pairs={{0,16},{1,17},{2,18},{3,19},{4,20},{5,21},{6,22},{7,23},{8,24},{9,... | collective-permute-start | bytes 221192 | tf_op jit(solution)/shard_map/ppermute | solution.py:194
  81.2 5.5 %collective-permute-start.6 = (bf16[9,32,128]{2,1,0:T(8,128)(2,1)S(1)}, bf16[9,32,128]{2,1,0:T(8,128)(2,1)S(1)}, u32[]{:S(2)}, u32[]{:S(2)}) collective-permute-start(bf16[9,32,128]{2,1,0:T(8,128)(2,1)S(1)} %get-tuple-element.23), channel_id=1, source_target_pairs={{0,16},{1,17},{2,18},{3,19},{4,20},{5,21},{6,22},{7,23},{8,24},{9,... | collective-permute-start | bytes 221192 | tf_op jit(solution)/shard_map/ppermute | solution.py:194
  87.9 18.5 %all-to-all-start.2 = ((bf16[8,2,9,32,128]{4,3,2,1,0:T(8,128)(2,1)}), bf16[8,2,9,32,128]{4,3,2,1,0:T(8,128)(2,1)}, u32[]{:S(2)}, u32[]{:S(2)}) async-start(bf16[8,2,9,32,128]{4,3,2,1,0:T(8,128)(2,1)} %broadcast_in_dim.5), calls=%async_computation.2 | async-start | bytes 2359296 | tf_op jit(solution)/shard_map/all_to_all | solution.py:189
  92.9 4.3 %collective-permute-start.8 = (bf16[1,32,256]{2,1,0:T(8,128)(2,1)S(1)}, bf16[1,32,256]{2,1,0:T(8,128)(2,1)S(1)}, u32[]{:S(2)}, u32[]{:S(2)}) collective-permute-start(bf16[1,32,256]{2,1,0:T(8,128)(2,1)S(1)} %get-tuple-element.30), channel_id=1, source_target_pairs={{1,0},{2,1},{3,2},{4,3},{5,4},{6,5},{7,6},{8,7},{9,8},{10,9},{11,1... | collective-permute-start | bytes 49160 | tf_op jit(solution)/shard_map/ppermute | solution.py:273
  94.2 3.9 %collective-permute-start.7 = (bf16[1,32,256]{2,1,0:T(8,128)(2,1)S(1)}, bf16[1,32,256]{2,1,0:T(8,128)(2,1)S(1)}, u32[]{:S(2)}, u32[]{:S(2)}) collective-permute-start(bf16[1,32,256]{2,1,0:T(8,128)(2,1)S(1)} %get-tuple-element.31), channel_id=1, source_target_pairs={{0,1},{1,2},{2,3},{3,4},{4,5},{5,6},{6,7},{7,8},{8,9},{9,10},{10,1... | collective-permute-start | bytes 49160 | tf_op jit(solution)/shard_map/ppermute | solution.py:272
  98.1 1.9 %copy-start.1 = (bf16[8,3,256,256]{3,2,1,0:T(8,128)(2,1)S(1)}, bf16[8,3,256,256]{3,2,1,0:T(8,128)(2,1)}, u32[]{:S(2)}) copy-start(bf16[8,3,256,256]{3,2,1,0:T(8,128)(2,1)} %near_ref.3) | copy-start | bytes 9437188
  100.0 0.9 copy-start.13
  101.5 0.7 copy-start.9
  106.4 6.2 %collective-permute-start.9 = (bf16[16,9,32,128]{3,2,1,0:T(8,128)(2,1)}, bf16[16,9,32,128]{3,2,1,0:T(8,128)(2,1)S(1)}, u32[]{:S(2)}, u32[]{:S(2)}) collective-permute-start(bf16[16,9,32,128]{3,2,1,0:T(8,128)(2,1)} %bitcast.6.own_ref), channel_id=1, source_target_pairs={{0,1},{1,0},{2,3},{3,2},{4,5},{5,4},{6,7},{7,6},{8,9},{9,8},{10,11... | collective-permute-start | bytes 3538952 | tf_op jit(solution)/shard_map/ppermute | solution.py:197
  119.6 2.9 %collective-permute-start.10 = (bf16[16,9,32,128]{3,2,1,0:T(8,128)(2,1)S(1)}, bf16[16,9,32,128]{3,2,1,0:T(8,128)(2,1)S(1)}, u32[]{:S(2)}, u32[]{:S(2)}) collective-permute-start(bf16[16,9,32,128]{3,2,1,0:T(8,128)(2,1)S(1)} %get-tuple-element.26), channel_id=1, source_target_pairs={{0,1},{1,0},{2,3},{3,2},{4,5},{5,4},{6,7},{7,6},{8,9},{9,8},{10,11... | collective-permute-start | bytes 3538952 | tf_op jit(solution)/shard_map/ppermute | solution.py:197
  143.2 6.3 %copy-start.6 = (bf16[8,96,96]{2,1,0:T(8,128)(2,1)S(1)}, bf16[8,96,96]{2,1,0:T(8,128)(2,1)}, u32[]{:S(2)}) copy-start(bf16[8,96,96]{2,1,0:T(8,128)(2,1)} %transfer_hbm.5) | copy-start | bytes 442372
  143.2 6.3 %copy-start.10 = (f32[8,32,256]{2,1,0:T(8,128)S(1)}, f32[8,32,256]{2,1,0:T(8,128)}, u32[]{:S(2)}) copy-start(f32[8,32,256]{2,1,0:T(8,128)} %copy-done.9) | copy-start | bytes 786436
  143.4 6.1 %collective-permute-start.11 = (bf16[1,9,32,128]{3,2,1,0:T(8,128)(2,1)S(1)}, bf16[1,9,32,128]{3,2,1,0:T(8,128)(2,1)S(1)}, u32[]{:S(2)}, u32[]{:S(2)}) collective-permute-start(bf16[1,9,32,128]{3,2,1,0:T(8,128)(2,1)S(1)} %get-tuple-element.28), channel_id=1, source_target_pairs={{0,16},{1,17},{2,18},{3,19},{4,20},{5,21},{6,22},{7,23},{8,24},{9,... | collective-permute-start | bytes 221192 | tf_op jit(solution)/shard_map/ppermute | solution.py:194

commit v4 on v3

--- a/solution.py
+++ b/solution.py
@@ -47,7 +47,7 @@
 
 
 def emit_coeffs(read_leaf, basis_ref, transfer_ref, ranks_ref, out_ref, leaves, rank_top):
-    mains, rhs, _ = out_ref.shape
+    copies, mains, rhs, _ = out_ref.shape
     lane = lax.broadcasted_iota(jnp.int32, (rhs, rank_top), 1)
     coeffs = []
     for i in range(leaves):
@@ -59,7 +59,9 @@
     wide = [widen(value.astype(F32)) for value in coeffs]
     for q in range(mains // 3):
         for k, tile in enumerate(packed(wide[3 * q : 3 * q + 3], wide[mains + q], rank_top)):
-            out_ref[3 * q + k] = tile.astype(BF)
+            tile = tile.astype(BF)
+            for c in range(copies):
+                out_ref[c, 3 * q + k] = tile
 
 
 def fetch(pairs, sems):
@@ -76,15 +78,16 @@
     emit_coeffs(lambda i: v_ref[i], basis_ref, transfer_ref, ranks_ref, out_ref, leaves, rank_top)
 
 
-def couple_kernel(source_ref, target_ref, own_ref, other_ref, coupling_ref, keep_ref, send_ref, sources, total, *, unroll):
+def couple_kernel(source_ref, target_ref, coupling_ref, *refs, sets, unroll):
+    in_refs, out_refs, (sources, total) = refs[:sets], refs[sets : 2 * sets], refs[2 * sets :]
     blocks, rank_top, _ = coupling_ref.shape
-    devices, mains, rhs, _ = own_ref.shape
+    chips, mains, rhs, _ = in_refs[0].shape
     quads = mains // 3
     clusters = mains + quads
 
     def split(d, _):
-        for half, packed_ref in enumerate((own_ref, other_ref)):
-            row = (half * devices + d) * clusters
+        for n, packed_ref in enumerate(in_refs):
+            row = (n * chips + d) * clusters
             tiles = [packed_ref[d, c] for c in range(mains)]
             for c in range(mains):
                 sources[row + c] = tiles[c]
@@ -95,7 +98,7 @@
                 total[row + c] = jnp.zeros((rhs, LANES), F32)
         return 0
 
-    lax.fori_loop(0, devices, split, 0, unroll=2)
+    lax.fori_loop(0, chips, split, 0)
 
     def some(s, _):
         for u in range(unroll):
@@ -108,60 +111,76 @@
     lax.fori_loop(0, blocks // unroll, some, 0)
 
     def pack(d, _):
-        for half, packed_ref in enumerate((keep_ref, send_ref)):
-            row = (half * devices + d) * clusters
+        for n, packed_ref in enumerate(out_refs):
+            row = (n * chips + d) * clusters
             for q in range(quads):
                 mains_now = [total[row + 3 * q + k] for k in range(3)]
                 for k, tile in enumerate(packed(mains_now, total[row + mains + q], rank_top)):
                     packed_ref[d, 3 * q + k] = tile.astype(BF)
         return 0
 
-    lax.fori_loop(0, devices, pack, 0, unroll=2)
-
-
-def near_kernel(v_ref, before_ref, after_ref, near_ref, out_ref):
+    lax.fori_loop(0, chips, pack, 0)
+
+
+def near_kernel(v_ref, near_ref, out_ref):
     leaves = v_ref.shape[0]
     for i in range(leaves):
-        left = v_ref[i - 1] if i > 0 else before_ref[0]
-        right = v_ref[i + 1] if i < leaves - 1 else after_ref[0]
-        out_ref[i] = dot(left, near_ref[i, 0]) + dot(v_ref[i], near_ref[i, 1]) + dot(right, near_ref[i, 2])
-
-
-def sum_kernel(parts_ref, keep_ref, send_ref):
-    parts, far, mains, _, _ = parts_ref.shape
-    for f in range(far):
-        for t in range(mains):
-            tile = parts_ref[0, f, t].astype(F32)
-            for p in range(1, parts):
-                tile = tile + parts_ref[p, f, t].astype(F32)
-            if f == 0:
-                keep_ref[t] = tile
-            else:
-                send_ref[f - 1, t] = tile.astype(BF)
-
-
-def field_kernel(ranks_ref, keep_ref, terms_ref, near_hbm, basis_hbm, transfer_hbm, out_ref, *rest):
-    *coeff_ref, near_ref, basis_ref, transfer_ref, sems = rest
-    copies = fetch([(transfer_hbm, transfer_ref), (basis_hbm, basis_ref), (near_hbm, near_ref)], sems)
+        total = dot(v_ref[i], near_ref[i, 1])
+        if i > 0:
+            total = total + dot(v_ref[i - 1], near_ref[i, 0])
+        if i < leaves - 1:
+            total = total + dot(v_ref[i + 1], near_ref[i, 2])
+        out_ref[i] = total
+
+
+def edge_kernel(before_ref, after_ref, first_ref, last_ref, out_ref):
+    out_ref[0] = dot(before_ref[0], first_ref[0, 0])
+    out_ref[1] = dot(after_ref[0], last_ref[0, 0])
+
+
+def part_sum(parts_ref, t):
+    tile = parts_ref[0, t].astype(F32)
+    for p in range(1, parts_ref.shape[0]):
+        tile = tile + parts_ref[p, t].astype(F32)
+    return tile
+
+
+def sum_kernel(parts_ref, out_ref):
+    for t in range(out_ref.shape[0]):
+        out_ref[t] = part_sum(parts_ref, t).astype(BF)
+
+
+def copy_kernel(in_ref, out_ref):
+    for t in range(in_ref.shape[0]):
+        tile = in_ref[t]
+        for c in range(out_ref.shape[0]):
+            out_ref[c, t] = tile
+
+
+def field_kernel(ranks_ref, near_ref, edge_ref, basis_ref, transfer_ref, parts_ref, *rest, away):
+    term_refs, out_ref, coeff_ref = rest[:away], rest[away], rest[away + 1 :]
     leaves, rank_top, _ = basis_ref.shape
-    parts, mains, rhs, _ = terms_ref.shape
+    _, mains, rhs, _ = parts_ref.shape
     tiles = []
     for t in range(mains):
-        tile = keep_ref[t]
-        for p in range(parts):
-            tile = tile + terms_ref[p, t].astype(F32)
+        tile = part_sum(parts_ref, t)
+        for term_ref in term_refs:
+            tile = tile + term_ref[t].astype(F32)
         tiles.append(tile)
     sums = tiles + [fourth(tiles[3 * q : 3 * q + 3], rank_top) for q in range(mains // 3)]
     lane = lax.broadcasted_iota(jnp.int32, (rhs, rank_top), 1)
     fields = [
         jnp.where(lane < ranks_ref[c], total[:, :rank_top], 0.0).astype(BF) for c, total in enumerate(sums)
     ]
-    for copy in copies:
-        copy.wait()
     for i in range(leaves):
         down = fields[i].astype(F32) + dot_t(fields[leaves + i // 2], transfer_ref[i])
         leaf_total = jnp.where(lane < ranks_ref[i], down, 0.0).astype(BF)
-        out_ref[i] = (near_ref[i] + dot(leaf_total, basis_ref[i])).astype(BF)
+        result = near_ref[i] + dot(leaf_total, basis_ref[i])
+        if i == 0:
+            result = result + edge_ref[0]
+        if i == leaves - 1:
+            result = result + edge_ref[1]
+        out_ref[i] = result.astype(BF)
     if coeff_ref:
         emit_coeffs(lambda i: out_ref[i], basis_ref, transfer_ref, ranks_ref, coeff_ref[0], leaves, rank_top)
 
@@ -203,28 +222,32 @@
         core = (device + me) % cores
         chip = (device // cores) % chips
         away = (sign * (device // cube - me // cube)) % far
-        return ((core * chips + chip) * far + away) * clusters + cluster % clusters
+        return ((core * far + away) * chips + chip) * clusters + cluster % clusters
 
     source_rows, target_rows = rows(block_source, -1), rows(block_target, 1)
 
     tile_shape = (mains, rhs, LANES)
     out_shape = shape((leaves, rhs, width), BF)
-    half_shape = shape((half,) + tile_shape, BF)
-    weights = [pltpu.VMEM(basis.shape, BF), pltpu.VMEM(transfer.shape, BF), pltpu.SemaphoreType.DMA((3,))]
+    part_shape = shape((chips,) + tile_shape, BF)
     first_coeffs = pl.pallas_call(
         coeff_kernel,
-        out_shape=shape(tile_shape, BF),
+        out_shape=part_shape,
         in_specs=[SMEM, HBM, HBM, HBM],
         out_specs=VMEM,
-        scratch_shapes=[pltpu.VMEM(charges.shape, BF)] + weights,
-        compiler_params=params(16),
+        scratch_shapes=[
+            pltpu.VMEM(charges.shape, BF),
+            pltpu.VMEM(basis.shape, BF),
+            pltpu.VMEM(transfer.shape, BF),
+            pltpu.SemaphoreType.DMA((3,)),
+        ],
     )(ranks, charges, basis, transfer)
 
+    sets = cores * far
     couple = pl.pallas_call(
-        functools.partial(couple_kernel, unroll=8),
-        out_shape=[half_shape, half_shape],
-        in_specs=[SMEM, SMEM, VMEM, VMEM, VMEM],
-        out_specs=[VMEM, VMEM],
+        functools.partial(couple_kernel, sets=sets, unroll=8),
+        out_shape=[part_shape] * sets,
+        in_specs=[SMEM, SMEM, VMEM] + [VMEM] * sets,
+        out_specs=[VMEM] * sets,
         scratch_shapes=[
             pltpu.VMEM((devices * clusters, rhs, LANES), BF),
             pltpu.VMEM((devices * clusters, rhs, LANES), F32),
@@ -238,7 +261,7 @@
     near = pl.pallas_call(
         near_kernel,
         out_shape=shape((leaves, rhs, width), F32),
-        in_specs=[VMEM] * 4,
+        in_specs=[VMEM] * 2,
         out_specs=VMEM,
         compiler_params=params(16),
         cost_estimate=pl.CostEstimate(
@@ -246,41 +269,56 @@
         ),
     )
 
+    edge = pl.pallas_call(
+        edge_kernel,
+        out_shape=shape((2, rhs, width), F32),
+        grid=(1,),
+        in_specs=[
+            VMEM,
+            VMEM,
+            pl.BlockSpec((1, 1, width, width), lambda i: (0, 0, 0, 0)),
+            pl.BlockSpec((1, 1, width, width), lambda i: (leaves - 1, 2, 0, 0)),
+        ],
+        out_specs=VMEM,
+        compiler_params=params(16),
+    )
+
     add_parts = pl.pallas_call(
-        sum_kernel,
-        out_shape=[shape(tile_shape, F32), shape((far - 1,) + tile_shape, BF)],
-        in_specs=[VMEM],
-        out_specs=[VMEM, VMEM],
-        compiler_params=params(16),
+        sum_kernel, out_shape=shape(tile_shape, BF), in_specs=[VMEM], out_specs=VMEM, compiler_params=params(16)
+    )
+    copies = pl.pallas_call(
+        copy_kernel, out_shape=part_shape, in_specs=[VMEM], out_specs=VMEM, compiler_params=params(16)
     )
 
     def finish(with_coeffs):
         return pl.pallas_call(
-            field_kernel,
-            out_shape=[out_shape, shape(tile_shape, BF)] if with_coeffs else [out_shape],
-            in_specs=[SMEM, VMEM, VMEM, HBM, HBM, HBM],
+            functools.partial(field_kernel, away=far - 1),
+            out_shape=[out_shape, part_shape] if with_coeffs else [out_shape],
+            in_specs=[SMEM] + [VMEM] * (4 + far),
             out_specs=[VMEM, VMEM] if with_coeffs else [VMEM],
-            scratch_shapes=[pltpu.VMEM((leaves, rhs, width), F32)] + weights,
             compiler_params=params(16),
         )
 
     ends = devices - 1
 
     def apply_matrix(field_in, coeffs, with_coeffs):
-        column = jnp.stack([coeffs] + [swap_far(coeffs, s) for s in range(1, far)])
-        own = exchange(jnp.broadcast_to(column[None], (chips,) + column.shape))
+        away = [swap_far(coeffs[0], s) for s in range(1, far)]
         before = lax.ppermute(field_in[leaves - 1 :], "clu", [(i, i + 1) for i in range(ends)])
         after = lax.ppermute(field_in[:1], "clu", [(i + 1, i) for i in range(ends)])
-        near_sum = near(field_in, before, after, near_field)
-        own, near_sum = lax.optimization_barrier((own, near_sum))
-        own = own.reshape(half_shape.shape)
-        other = swap_cores(own)
-        keep, send = couple(source_rows, target_rows, own, other, coupling)
-        chip_sum = keep.astype(F32) + swap_cores(send).astype(F32)
-        parts = exchange(chip_sum.astype(BF).reshape((chips, far) + tile_shape))
-        mine, away = add_parts(parts)
-        terms = jnp.concatenate([swap_far(away[s - 1 : s], s) for s in range(1, far)])
-        return finish(with_coeffs)(ranks, mine, terms, near_sum, basis, transfer)
+        own = [exchange(coeffs)]
+        own += [exchange(copies(part)) for part in away]
+        near_sum = near(field_in, near_field)
+        edges = edge(before, after, near_field, near_field)
+        own[-1], near_sum, edges = lax.optimization_barrier((own[-1], near_sum, edges))
+        other = [swap_cores(part) for part in own]
+        totals = couple(source_rows, target_rows, coupling, *own, *other)
+        terms = []
+        for s in list(range(1, far)) + [0]:
+            chip_sum = totals[s].astype(F32) + swap_cores(totals[far + s]).astype(F32)
+            parts = exchange(chip_sum.astype(BF))
+            if s:
+                terms.append(swap_far(add_parts(parts), s))
+        return finish(with_coeffs)(ranks, near_sum, edges, basis, transfer, parts, *terms)
 
     first, second_coeffs = apply_matrix(charges, first_coeffs, True)
     (second,) = apply_matrix(first, second_coeffs, False)

time: 153 us -> 170 us (1.11)
  blocking collectives: 41.3 us -> 0 us
  starting transfers between devices: 33.5 us -> 61.4 us
  waiting for transfers between devices: 38 us -> 49.9 us
  local copies, waits for them, and re-layouts: 14.5 us -> 24.4 us
  other arithmetic: 0.69 us -> 5.05 us
  Pallas kernels: 23.6 us -> 26.7 us
    all_to_all x2 -> x0, blocking collectives: 41.3 us -> none  [exchange(): lax.all_to_all(parts, 'clu', split_axis=0, concat_axis=0, tiled=True, axi...]
    all_to_all x2 -> x8, starting transfers between devices: 8.63 us -> 37.6 us  [exchange(): lax.all_to_all(parts, 'clu', split_axis=0, concat_axis=0, tiled=True, axi...]
    all_to_all x2 -> x8, waiting for transfers between devices: 13.4 us -> 31.9 us  [exchange(): lax.all_to_all(parts, 'clu', split_axis=0, concat_axis=0, tiled=True, axi...]
    unnamed x37 -> x57, local copies, waits for them, and re-layouts: 11.3 us -> 21.8 us
    ppermute x4, waiting for transfers between devices: 14.9 us -> 8.81 us  [swap_far(): lax.ppermute(part, 'clu', [(d, (d + shift * cube) % devices) for d in ran...]
    convert_element_type x2 -> x4, other arithmetic: 0.62 us -> 5.01 us  [apply_matrix(): parts = exchange(chip_sum.astype(BF))]
    pallas_call x9 -> x13, Pallas kernels: 23.6 us -> 26.7 us  [the longest x2 14.3 us: apply_matrix(): totals = couple(source_rows, target_rows, coupling, *own, *other)]
    broadcast_in_dim x2 -> x0, local copies, waits for them, and re-layouts: 2.47 us -> none  [apply_matrix(): own = exchange(jnp.broadcast_to(column[None], (chips,) + column.shape))]
  transfers between devices with their start and end apart: 14 -> 24, of which waited for: 11 -> 13; matrix products, arithmetic and copies ran while one was open for 3% -> 6% of each run, Pallas kernels for 1% -> 2%
where the time goes in v4:
time: 170 us; the launch traced here: 168 us
  starting transfers between devices  61.4 us (36%)
  waiting for transfers between devices  49.9 us (29%)
  Pallas kernels  26.7 us (16%)
  local copies, waits for them, and re-layouts  24.4 us (14%)
  other arithmetic  5.05 us (3%)
    all_to_all x8, starting transfers between devices, exchange(): lax.all_to_all(parts, 'clu', split_axis=0, concat_axis=0, tiled=True, axi...  37.6 us
    all_to_all x8, waiting for transfers between devices, exchange(): lax.all_to_all(parts, 'clu', split_axis=0, concat_axis=0, tiled=True, axi...  31.9 us
    unnamed x57, local copies, waits for them, and re-layouts  21.8 us
    pallas_call x2, Pallas kernels, apply_matrix(): totals = couple(source_rows, target_rows, coupling, *own, *other)  14.3 us
    ppermute x4, starting transfers between devices, swap_far(): lax.ppermute(part, 'clu', [(d, (d + shift * cube) % devices) for d in ran...  10.6 us
    ppermute x8, waiting for transfers between devices, swap_cores(): return lax.ppermute(part, 'clu', [(d, d ^ 1) for d in range(devices)])  9.25 us
    ppermute x4, waiting for transfers between devices, swap_far(): lax.ppermute(part, 'clu', [(d, (d + shift * cube) % devices) for d in ran...  8.81 us
    ppermute x2, starting transfers between devices, apply_matrix(): lax.ppermute(field_in[leaves - 1:], 'clu', [(i, i + 1) for i in range(end...  6.06 us
  transfers between devices with their start and end apart: 24, of which 13 were waited for; matrix products, arithmetic and copies ran while one was open for 6% of the time, Pallas kernels for 2%

profile of v4, /device:TPU:0, one launch (start us, length us, event | category | flops | bytes accessed | tf_op | source)
XLA Modules:
  0.0 168.3 jit_solution(2794051679661171516)
XLA Ops:
  0.6 3.2 %shard_map.95 = bf16[8,9,32,128]{3,2,1,0:T(8,128)(2,1)} custom-call(s32[12]{0:T(128)} %ranks_ref.5, bf16[8,32,256]{2,1,0:T(8,128)(2,1)} %v_ref.1, bf16[8,96,256]{2,1,0:T(8,128)(2,1)} %basis_ref.3, bf16[8,96,96]{2,1,0:T(8,128)(2,1)} %transfer_ref.3), custom_call_target="tpu_custom_call" | custom-call | tf_op jit(solution)/shard_map/pallas_call | solution.py:232
  3.9 6.5 %all-to-all-start.1 = ((bf16[8,9,32,128]{3,2,1,0:T(8,128)(2,1)}), bf16[8,9,32,128]{3,2,1,0:T(8,128)(2,1)}, u32[]{:S(2)}, u32[]{:S(2)}) async-start(bf16[8,9,32,128]{3,2,1,0:T(8,128)(2,1)} %shard_map.95), calls=%async_computation.1 | async-start | bytes 1179648 | tf_op jit(solution)/shard_map/all_to_all | solution.py:208
  10.3 0.9 slice_bitcast_fusion
  11.2 2.6 %collective-permute-start = (bf16[9,32,128]{2,1,0:T(8,128)(2,1)S(1)}, bf16[9,32,128]{2,1,0:T(8,128)(2,1)S(1)}, u32[]{:S(2)}, u32[]{:S(2)}) collective-permute-start(bf16[9,32,128]{2,1,0:T(8,128)(2,1)S(1)} %slice_bitcast_fusion), channel_id=1, source_target_pairs={{0,16},{1,17},{2,18},{3,19},{4,20},{5,21},{6,22},{7,23},{8,24},{9,... | collective-permute-start | bytes 221192 | tf_op jit(solution)/shard_map/ppermute | solution.py:213
  13.8 4.6 %collective-permute-done.in_ref = bf16[9,32,128]{2,1,0:T(8,128)(2,1)S(1)} collective-permute-done((bf16[9,32,128]{2,1,0:T(8,128)(2,1)S(1)}, bf16[9,32,128]{2,1,0:T(8,128)(2,1)S(1)}, u32[]{:S(2)}, u32[]{:S(2)}) %collective-permute-start) | collective-permute-done | bytes 73760 | tf_op jit(solution)/shard_map/ppermute | solution.py:213
  18.5 0.8 copy-done.5
  19.3 2.4 %all-to-all-done.1.refs_0_ = bf16[8,9,32,128]{3,2,1,0:T(8,128)(2,1)} async-done(((bf16[8,9,32,128]{3,2,1,0:T(8,128)(2,1)}), bf16[8,9,32,128]{3,2,1,0:T(8,128)(2,1)}, u32[]{:S(2)}, u32[]{:S(2)}) %all-to-all-start.1) | async-done | bytes 589856 | tf_op jit(solution)/shard_map/all_to_all | solution.py:208
  21.7 5.5 %all-to-all-start = ((bf16[8,9,32,128]{3,2,1,0:T(8,128)(2,1)}), bf16[8,9,32,128]{3,2,1,0:T(8,128)(2,1)}, u32[]{:S(2)}, u32[]{:S(2)}) async-start(bf16[8,9,32,128]{3,2,1,0:T(8,128)(2,1)} %copy-done.5), calls=%async_computation | async-start | bytes 1179648 | tf_op jit(solution)/shard_map/all_to_all | solution.py:208
  27.2 1.3 collective-permute-start.2
  28.5 3.0 %collective-permute-start.1 = (bf16[1,32,256]{2,1,0:T(8,128)(2,1)S(1)}, bf16[1,32,256]{2,1,0:T(8,128)(2,1)S(1)}, u32[]{:S(2)}, u32[]{:S(2)}) collective-permute-start(bf16[1,32,256]{2,1,0:T(8,128)(2,1)S(1)} %get-tuple-element.37), channel_id=1, source_target_pairs={{0,1},{1,2},{2,3},{3,4},{4,5},{5,6},{6,7},{7,8},{8,9},{9,10},{10,1... | collective-permute-start | bytes 49160 | tf_op jit(solution)/shard_map/ppermute | solution.py:306
  31.6 0.6 shard_map.97.near_ref
  32.2 0.7 copy-done.10
  33.0 0.6 copy-done.19
  33.7 2.0 %collective-permute-start.3 = (bf16[8,9,32,128]{3,2,1,0:T(8,128)(2,1)}, bf16[8,9,32,128]{3,2,1,0:T(8,128)(2,1)}, u32[]{:S(2)}, u32[]{:S(2)}) collective-permute-start(bf16[8,9,32,128]{3,2,1,0:T(8,128)(2,1)} %all-to-all-done.1.refs_0_), channel_id=1, source_target_pairs={{0,1},{1,0},{2,3},{3,2},{4,5},{5,4},{6,7},{7,6},{8,9},{9,8},{10,11... | collective-permute-start | bytes 1769480 | tf_op jit(solution)/shard_map/ppermute | solution.py:216
  35.7 4.8 %copy.10.coupling_ref = bf16[128,96,96]{2,1,0:T(8,128)(2,1)} copy(bf16[128,96,96]{0,2,1:T(8,128)(2,1)} %param.12) | data formatting | bytes 4718592 | tf_op args[4]
  40.6 1.9 %copy-done.1 = bf16[128,96,96]{2,1,0:T(8,128)(2,1)S(1)} copy-done((bf16[128,96,96]{2,1,0:T(8,128)(2,1)S(1)}, bf16[128,96,96]{2,1,0:T(8,128)(2,1)}, u32[]{:S(2)}) %copy-start.1) | copy-done | bytes 2359320
  42.5 7.3 %shard_map.99 = (bf16[8,9,32,128]{3,2,1,0:T(8,128)(2,1)S(1)}, bf16[8,9,32,128]{3,2,1,0:T(8,128)(2,1)S(1)}, bf16[8,9,32,128]{3,2,1,0:T(8,128)(2,1)S(1)}, bf16[8,9,32,128]{3,2,1,0:T(8,128)(2,1)S(1)}) custom-call(s32[128]{0:T(128)S(1)} %get-tuple-element.38.source_ref, s32[128]{0:T(128)S(1)} %get-tuple-element.39.target_ref, ...), custom_call_target="tpu_custom_call" | custom-call | flops 75497472 | bytes 10485760 | tf_op jit(solution)/shard_map/pallas_call | solution.py:314
  49.8 0.8 copy-done.18
  50.6 0.9 copy-done.25
  52.0 1.6 collective-permute-done.6
  53.6 1.0 add_convert_fusion.2
  54.6 4.8 %all-to-all-start.3 = ((bf16[8,9,32,128]{3,2,1,0:T(8,128)(2,1)}), bf16[8,9,32,128]{3,2,1,0:T(8,128)(2,1)}, u32[]{:S(2)}, u32[]{:S(2)}) async-start(bf16[8,9,32,128]{3,2,1,0:T(8,128)(2,1)} %add_convert_fusion.2), calls=%async_computation.3 | async-start | bytes 1179648 | tf_op jit(solution)/shard_map/all_to_all | solution.py:208
  59.4 2.2 %collective-permute-done.5 = bf16[8,9,32,128]{3,2,1,0:T(8,128)(2,1)S(1)} collective-permute-done((bf16[8,9,32,128]{3,2,1,0:T(8,128)(2,1)}, bf16[8,9,32,128]{3,2,1,0:T(8,128)(2,1)S(1)}, u32[]{:S(2)}, u32[]{:S(2)}) %collective-permute-start.5) | collective-permute-done | bytes 589856 | tf_op jit(solution)/shard_map/ppermute | solution.py:216
  61.6 2.1 %add_convert_fusion.3 = bf16[8,9,32,128]{3,2,1,0:T(8,128)(2,1)} fusion(bf16[8,9,32,128]{3,2,1,0:T(8,128)(2,1)S(1)} %collective-permute-done.5, bf16[8,9,32,128]{3,2,1,0:T(8,128)(2,1)} %copy-done.18), kind=kLoop, calls=%fused_computation.3 | loop fusion | flops 1179648 | bytes 1769472 | tf_op jit(solution)/shard_map/convert_element_type | solution.py:318
  63.7 6.2 %all-to-all-done.3.parts_ref = bf16[8,9,32,128]{3,2,1,0:T(8,128)(2,1)} async-done(((bf16[8,9,32,128]{3,2,1,0:T(8,128)(2,1)}), bf16[8,9,32,128]{3,2,1,0:T(8,128)(2,1)}, u32[]{:S(2)}, u32[]{:S(2)}) %all-to-all-start.3) | async-done | bytes 589856 | tf_op jit(solution)/shard_map/all_to_all | solution.py:208
  69.8 4.2 %all-to-all-start.2 = ((bf16[8,9,32,128]{3,2,1,0:T(8,128)(2,1)}), bf16[8,9,32,128]{3,2,1,0:T(8,128)(2,1)}, u32[]{:S(2)}, u32[]{:S(2)}) async-start(bf16[8,9,32,128]{3,2,1,0:T(8,128)(2,1)} %add_convert_fusion.3), calls=%async_computation.2 | async-start | bytes 1179648 | tf_op jit(solution)/shard_map/all_to_all | solution.py:208
  74.0 1.8 %shard_map.100 = bf16[9,32,128]{2,1,0:T(8,128)(2,1)} custom-call(bf16[8,9,32,128]{3,2,1,0:T(8,128)(2,1)} %all-to-all-done.3.parts_ref), custom_call_target="tpu_custom_call" | custom-call | tf_op jit(solution)/shard_map/pallas_call | solution.py:320
  75.8 3.4 %collective-permute-start.7 = (bf16[9,32,128]{2,1,0:T(8,128)(2,1)}, bf16[9,32,128]{2,1,0:T(8,128)(2,1)}, u32[]{:S(2)}, u32[]{:S(2)}) collective-permute-start(bf16[9,32,128]{2,1,0:T(8,128)(2,1)} %shard_map.100), channel_id=1, source_target_pairs={{0,16},{1,17},{2,18},{3,19},{4,20},{5,21},{6,22},{7,23},{8,24},{9,... | collective-permute-start | bytes 221192 | tf_op jit(solution)/shard_map/ppermute | solution.py:213
  79.2 6.2 %all-to-all-done.2.parts_ref = bf16[8,9,32,128]{3,2,1,0:T(8,128)(2,1)} async-done(((bf16[8,9,32,128]{3,2,1,0:T(8,128)(2,1)}), bf16[8,9,32,128]{3,2,1,0:T(8,128)(2,1)}, u32[]{:S(2)}, u32[]{:S(2)}) %all-to-all-start.2) | async-done | bytes 589856 | tf_op jit(solution)/shard_map/all_to_all | solution.py:208
  85.5 0.9 copy-done.6
  86.4 0.9 copy-done.11
  87.3 0.8 copy-done.20
  88.2 3.2 %shard_map.101 = (bf16[8,32,256]{2,1,0:T(8,128)(2,1)}, bf16[8,9,32,128]{3,2,1,0:T(8,128)(2,1)S(1)}) custom-call(s32[12]{0:T(128)S(1)} %copy-done.24, f32[8,32,256]{2,1,0:T(8,128)S(1)} %copy-done.11, f32[2,32,256]{2,1,0:T(8,128)S(1)} %copy-done.20, bf16[8,96,256]{2,1,0:T(8,128)(2,1)S(1)} %copy-done.3, bf16[8,96,96]{2,1,0:T(8,128)(2,1)S(1)} %copy-done.6, ...), custom_call_target="tpu_custom_call" | custom-call | tf_op jit(solution)/shard_map/pallas_call | solution.py:321
  91.4 0.8 copy-done.12
  92.2 4.3 %all-to-all-start.5 = ((bf16[8,9,32,128]{3,2,1,0:T(8,128)(2,1)}), bf16[8,9,32,128]{3,2,1,0:T(8,128)(2,1)}, u32[]{:S(2)}, u32[]{:S(2)}) async-start(bf16[8,9,32,128]{3,2,1,0:T(8,128)(2,1)} %copy-done.12), calls=%async_computation.5 | async-start | bytes 1179648 | tf_op jit(solution)/shard_map/all_to_all | solution.py:208
  96.5 0.9 slice_bitcast_fusion.1
  97.4 1.7 %collective-permute-start.8 = (bf16[9,32,128]{2,1,0:T(8,128)(2,1)S(1)}, bf16[9,32,128]{2,1,0:T(8,128)(2,1)S(1)}, u32[]{:S(2)}, u32[]{:S(2)}) collective-permute-start(bf16[9,32,128]{2,1,0:T(8,128)(2,1)S(1)} %slice_bitcast_fusion.1), channel_id=1, source_target_pairs={{0,16},{1,17},{2,18},{3,19},{4,20},{5,21},{6,22},{7,23},{8,24},{9,... | collective-permute-start | bytes 221192 | tf_op jit(solution)/shard_map/ppermute | solution.py:213
  99.0 4.2 %collective-permute-done.8.in_ref = bf16[9,32,128]{2,1,0:T(8,128)(2,1)S(1)} collective-permute-done((bf16[9,32,128]{2,1,0:T(8,128)(2,1)S(1)}, bf16[9,32,128]{2,1,0:T(8,128)(2,1)S(1)}, u32[]{:S(2)}, u32[]{:S(2)}) %collective-permute-start.8) | collective-permute-done | bytes 73760 | tf_op jit(solution)/shard_map/ppermute | solution.py:213
  103.4 0.8 copy-done.4
  104.2 2.1 %all-to-all-done.5.refs_0_ = bf16[8,9,32,128]{3,2,1,0:T(8,128)(2,1)} async-done(((bf16[8,9,32,128]{3,2,1,0:T(8,128)(2,1)}), bf16[8,9,32,128]{3,2,1,0:T(8,128)(2,1)}, u32[]{:S(2)}, u32[]{:S(2)}) %all-to-all-start.5) | async-done | bytes 589856 | tf_op jit(solution)/shard_map/all_to_all | solution.py:208
  106.3 4.4 %all-to-all-start.4 = ((bf16[8,9,32,128]{3,2,1,0:T(8,128)(2,1)}), bf16[8,9,32,128]{3,2,1,0:T(8,128)(2,1)}, u32[]{:S(2)}, u32[]{:S(2)}) async-start(bf16[8,9,32,128]{3,2,1,0:T(8,128)(2,1)} %copy-done.4), calls=%async_computation.4 | async-start | bytes 1179648 | tf_op jit(solution)/shard_map/all_to_all | solution.py:208
  110.7 0.7 fusion.14
  111.4 1.3 collective-permute-start.10
  112.7 3.0 %collective-permute-start.9 = (bf16[1,32,256]{2,1,0:T(8,128)(2,1)S(1)}, bf16[1,32,256]{2,1,0:T(8,128)(2,1)S(1)}, u32[]{:S(2)}, u32[]{:S(2)}) collective-permute-start(bf16[1,32,256]{2,1,0:T(8,128)(2,1)S(1)} %get-tuple-element.35), channel_id=1, source_target_pairs={{0,1},{1,2},{2,3},{3,4},{4,5},{5,6},{6,7},{7,8},{8,9},{9,10},{10,1... | collective-permute-start | bytes 49160 | tf_op jit(solution)/shard_map/ppermute | solution.py:306
  115.8 0.9 copy-done.23
  117.3 0.7 copy-done.8
  118.1 0.6 copy-done.21
  118.8 1.7 collective-permute-start.11
  120.4 1.8 %collective-permute-done.11.refs_2_ = bf16[8,9,32,128]{3,2,1,0:T(8,128)(2,1)S(1)} collective-permute-done((bf16[8,9,32,128]{3,2,1,0:T(8,128)(2,1)}, bf16[8,9,32,128]{3,2,1,0:T(8,128)(2,1)S(1)}, u32[]{:S(2)}, u32[]{:S(2)}) %collective-permute-start.11) | collective-permute-done | bytes 589856 | tf_op jit(solution)/shard_map/ppermute | solution.py:216
  122.3 0.9 copy-done.14
  123.1 1.9 %copy-done.2 = bf16[128,96,96]{2,1,0:T(8,128)(2,1)S(1)} copy-done((bf16[128,96,96]{2,1,0:T(8,128)(2,1)S(1)}, bf16[128,96,96]{2,1,0:T(8,128)(2,1)}, u32[]{:S(2)}) %copy-start.2) | copy-done | bytes 2359320
  125.0 1.1 copy-done.15
  126.1 7.0 %shard_map.105 = (bf16[8,9,32,128]{3,2,1,0:T(8,128)(2,1)S(1)}, bf16[8,9,32,128]{3,2,1,0:T(8,128)(2,1)S(1)}, bf16[8,9,32,128]{3,2,1,0:T(8,128)(2,1)S(1)}, bf16[8,9,32,128]{3,2,1,0:T(8,128)(2,1)S(1)}) custom-call(s32[128]{0:T(128)S(1)} %get-tuple-element.38.source_ref, s32[128]{0:T(128)S(1)} %get-tuple-element.39.target_ref, ...), custom_call_target="tpu_custom_call" | custom-call | flops 75497472 | bytes 10485760 | tf_op jit(solution)/shard_map/pallas_call | solution.py:314
  133.1 0.8 copy-done.16
  134.2 1.6 collective-permute-done.14
  135.9 1.0 add_convert_fusion
  136.9 4.5 %all-to-all-start.7 = ((bf16[8,9,32,128]{3,2,1,0:T(8,128)(2,1)}), bf16[8,9,32,128]{3,2,1,0:T(8,128)(2,1)S(1)}, u32[]{:S(2)}, u32[]{:S(2)}) async-start(bf16[8,9,32,128]{3,2,1,0:T(8,128)(2,1)} %add_convert_fusion), calls=%async_computation.7 | async-start | bytes 1179648 | tf_op jit(solution)/shard_map/all_to_all | solution.py:208
  141.4 1.9 %collective-permute-done.13 = bf16[8,9,32,128]{3,2,1,0:T(8,128)(2,1)S(1)} collective-permute-done((bf16[8,9,32,128]{3,2,1,0:T(8,128)(2,1)S(1)}, bf16[8,9,32,128]{3,2,1,0:T(8,128)(2,1)S(1)}, u32[]{:S(2)}, u32[]{:S(2)}) %collective-permute-start.13) | collective-permute-done | bytes 589856 | tf_op jit(solution)/shard_map/ppermute | solution.py:216
  143.3 1.0 add_convert_fusion.1
  144.3 7.2 %all-to-all-done.7.parts_ref = bf16[8,9,32,128]{3,2,1,0:T(8,128)(2,1)S(1)} async-done(((bf16[8,9,32,128]{3,2,1,0:T(8,128)(2,1)}), bf16[8,9,32,128]{3,2,1,0:T(8,128)(2,1)S(1)}, u32[]{:S(2)}, u32[]{:S(2)}) %all-to-all-start.7) | async-done | bytes 589856 | tf_op jit(solution)/shard_map/all_to_all | solution.py:208
  151.5 3.5 %all-to-all-start.6 = ((bf16[8,9,32,128]{3,2,1,0:T(8,128)(2,1)}), bf16[8,9,32,128]{3,2,1,0:T(8,128)(2,1)S(1)}, u32[]{:S(2)}, u32[]{:S(2)}) async-start(bf16[8,9,32,128]{3,2,1,0:T(8,128)(2,1)} %add_convert_fusion.1), calls=%async_computation.6 | async-start | bytes 1179648 | tf_op jit(solution)/shard_map/all_to_all | solution.py:208
  155.2 2.9 %collective-permute-start.15 = (bf16[9,32,128]{2,1,0:T(8,128)(2,1)S(1)}, bf16[9,32,128]{2,1,0:T(8,128)(2,1)S(1)}, u32[]{:S(2)}, u32[]{:S(2)}) collective-permute-start(bf16[9,32,128]{2,1,0:T(8,128)(2,1)S(1)} %shard_map.106), channel_id=1, source_target_pairs={{0,16},{1,17},{2,18},{3,19},{4,20},{5,21},{6,22},{7,23},{8,24},{9,... | collective-permute-start | bytes 221192 | tf_op jit(solution)/shard_map/ppermute | solution.py:213
  158.1 7.8 %all-to-all-done.6.parts_ref = bf16[8,9,32,128]{3,2,1,0:T(8,128)(2,1)S(1)} async-done(((bf16[8,9,32,128]{3,2,1,0:T(8,128)(2,1)}), bf16[8,9,32,128]{3,2,1,0:T(8,128)(2,1)S(1)}, u32[]{:S(2)}, u32[]{:S(2)}) %all-to-all-start.6) | async-done | bytes 589856 | tf_op jit(solution)/shard_map/all_to_all | solution.py:208
  165.9 2.5 %shard_map.107 = bf16[8,32,256]{2,1,0:T(8,128)(2,1)} custom-call(s32[12]{0:T(128)S(1)} %copy-done.24, f32[8,32,256]{2,1,0:T(8,128)S(1)} %copy-done.9, f32[2,32,256]{2,1,0:T(8,128)S(1)} %copy-done.22, bf16[8,96,256]{2,1,0:T(8,128)(2,1)S(1)} %copy-done.3, bf16[8,96,96]{2,1,0:T(8,128)(2,1)S(1)} %copy-done.7, ...), custom_call_target="tpu_custom_call" | custom-call | tf_op jit(solution)/shard_map/pallas_call | solution.py:321
  (63 shorter events, 2.2 us)
Async XLA Ops:
  0.6 26.6 %copy-start.13 = (bf16[8,32,256]{2,1,0:T(8,128)(2,1)S(1)}, bf16[8,32,256]{2,1,0:T(8,128)(2,1)}, u32[]{:S(2)}) copy-start(bf16[8,32,256]{2,1,0:T(8,128)(2,1)} %v_ref.1) | copy-start | bytes 393220
  3.9 27.7 %copy-start = (bf16[8,3,256,256]{3,2,1,0:T(8,128)(2,1)S(1)}, bf16[8,3,256,256]{3,2,1,0:T(8,128)(2,1)}, u32[]{:S(2)}) copy-start(bf16[8,3,256,256]{3,2,1,0:T(8,128)(2,1)} %last_ref.3) | copy-start | bytes 9437188
  3.9 17.8 %all-to-all-start.1 = ((bf16[8,9,32,128]{3,2,1,0:T(8,128)(2,1)}), bf16[8,9,32,128]{3,2,1,0:T(8,128)(2,1)}, u32[]{:S(2)}, u32[]{:S(2)}) async-start(bf16[8,9,32,128]{3,2,1,0:T(8,128)(2,1)} %shard_map.95), calls=%async_computation.1 | async-start | bytes 1179648 | tf_op jit(solution)/shard_map/all_to_all | solution.py:208
  11.2 7.2 %collective-permute-start = (bf16[9,32,128]{2,1,0:T(8,128)(2,1)S(1)}, bf16[9,32,128]{2,1,0:T(8,128)(2,1)S(1)}, u32[]{:S(2)}, u32[]{:S(2)}) collective-permute-start(bf16[9,32,128]{2,1,0:T(8,128)(2,1)S(1)} %slice_bitcast_fusion), channel_id=1, source_target_pairs={{0,16},{1,17},{2,18},{3,19},{4,20},{5,21},{6,22},{7,23},{8,24},{9,... | collective-permute-start | bytes 221192 | tf_op jit(solution)/shard_map/ppermute | solution.py:213
  18.5 0.8 copy-start.5
  21.7 14.0 %all-to-all-start = ((bf16[8,9,32,128]{3,2,1,0:T(8,128)(2,1)}), bf16[8,9,32,128]{3,2,1,0:T(8,128)(2,1)}, u32[]{:S(2)}, u32[]{:S(2)}) async-start(bf16[8,9,32,128]{3,2,1,0:T(8,128)(2,1)} %copy-done.5), calls=%async_computation | async-start | bytes 1179648 | tf_op jit(solution)/shard_map/all_to_all | solution.py:208
  27.2 5.7 %collective-permute-start.2 = (bf16[1,32,256]{2,1,0:T(8,128)(2,1)S(1)}, bf16[1,32,256]{2,1,0:T(8,128)(2,1)S(1)}, u32[]{:S(2)}, u32[]{:S(2)}) collective-permute-start(bf16[1,32,256]{2,1,0:T(8,128)(2,1)S(1)} %get-tuple-element.36), channel_id=1, source_target_pairs={{1,0},{2,1},{3,2},{4,3},{5,4},{6,5},{7,6},{8,7},{9,8},{10,9},{11,1... | collective-permute-start | bytes 49160 | tf_op jit(solution)/shard_map/ppermute | solution.py:307
  28.5 4.4 %collective-permute-start.1 = (bf16[1,32,256]{2,1,0:T(8,128)(2,1)S(1)}, bf16[1,32,256]{2,1,0:T(8,128)(2,1)S(1)}, u32[]{:S(2)}, u32[]{:S(2)}) collective-permute-start(bf16[1,32,256]{2,1,0:T(8,128)(2,1)S(1)} %get-tuple-element.37), channel_id=1, source_target_pairs={{0,1},{1,2},{2,3},{3,4},{4,5},{5,6},{6,7},{7,8},{8,9},{9,10},{10,1... | collective-permute-start | bytes 49160 | tf_op jit(solution)/shard_map/ppermute | solution.py:306
  32.2 0.7 copy-start.10
  33.0 0.6 copy-start.19
  33.7 6.9 %collective-permute-start.3 = (bf16[8,9,32,128]{3,2,1,0:T(8,128)(2,1)}, bf16[8,9,32,128]{3,2,1,0:T(8,128)(2,1)}, u32[]{:S(2)}, u32[]{:S(2)}) collective-permute-start(bf16[8,9,32,128]{3,2,1,0:T(8,128)(2,1)} %all-to-all-done.1.refs_0_), channel_id=1, source_target_pairs={{0,1},{1,0},{2,3},{3,2},{4,5},{5,4},{6,7},{7,6},{8,9},{9,8},{10,11... | collective-permute-start | bytes 1769480 | tf_op jit(solution)/shard_map/ppermute | solution.py:216
  35.7 4.9 %collective-permute-start.4 = (bf16[8,9,32,128]{3,2,1,0:T(8,128)(2,1)}, bf16[8,9,32,128]{3,2,1,0:T(8,128)(2,1)}, u32[]{:S(2)}, u32[]{:S(2)}) collective-permute-start(bf16[8,9,32,128]{3,2,1,0:T(8,128)(2,1)} %all-to-all-done.refs_1_), channel_id=1, source_target_pairs={{0,1},{1,0},{2,3},{3,2},{4,5},{5,4},{6,7},{7,6},{8,9},{9,8},{10,11... | collective-permute-start | bytes 1769480 | tf_op jit(solution)/shard_map/ppermute | solution.py:216
  35.7 4.8 %copy-start.26 = (s32[128]{0:T(128)S(1)}, s32[128]{0:T(128)}, u32[]{:S(2)}) copy-start(s32[128]{0:T(128)} %param.14) | copy-start | bytes 1540
  35.7 4.8 %copy-start.27 = (s32[128]{0:T(128)S(1)}, s32[128]{0:T(128)}, u32[]{:S(2)}) copy-start(s32[128]{0:T(128)} %param.15) | copy-start | bytes 1540
  40.6 1.9 %copy-start.1 = (bf16[128,96,96]{2,1,0:T(8,128)(2,1)S(1)}, bf16[128,96,96]{2,1,0:T(8,128)(2,1)}, u32[]{:S(2)}) copy-start(bf16[128,96,96]{2,1,0:T(8,128)(2,1)} %copy.10.coupling_ref) | copy-start | bytes 7077892
  49.8 0.8 copy-start.18
  50.6 0.9 copy-start.25
  51.5 2.1 %collective-permute-start.6 = (bf16[8,9,32,128]{3,2,1,0:T(8,128)(2,1)S(1)}, bf16[8,9,32,128]{3,2,1,0:T(8,128)(2,1)S(1)}, u32[]{:S(2)}, u32[]{:S(2)}) collective-permute-start(bf16[8,9,32,128]{3,2,1,0:T(8,128)(2,1)S(1)} %get-tuple-element.24), channel_id=1, source_target_pairs={{0,1},{1,0},{2,3},{3,2},{4,5},{5,4},{6,7},{7,6},{8,9},{9,8},{10,11... | collective-permute-start | bytes 1769480 | tf_op jit(solution)/shard_map/ppermute | solution.py:216
  54.6 15.2 %all-to-all-start.3 = ((bf16[8,9,32,128]{3,2,1,0:T(8,128)(2,1)}), bf16[8,9,32,128]{3,2,1,0:T(8,128)(2,1)}, u32[]{:S(2)}, u32[]{:S(2)}) async-start(bf16[8,9,32,128]{3,2,1,0:T(8,128)(2,1)} %add_convert_fusion.2), calls=%async_computation.3 | async-start | bytes 1179648 | tf_op jit(solution)/shard_map/all_to_all | solution.py:208
  59.4 2.2 %collective-permute-start.5 = (bf16[8,9,32,128]{3,2,1,0:T(8,128)(2,1)}, bf16[8,9,32,128]{3,2,1,0:T(8,128)(2,1)S(1)}, u32[]{:S(2)}, u32[]{:S(2)}) collective-permute-start(bf16[8,9,32,128]{3,2,1,0:T(8,128)(2,1)} %copy-done.25), channel_id=1, source_target_pairs={{0,1},{1,0},{2,3},{3,2},{4,5},{5,4},{6,7},{7,6},{8,9},{9,8},{10,11... | collective-permute-start | bytes 1769480 | tf_op jit(solution)/shard_map/ppermute | solution.py:216
  63.7 21.8 %copy-start.3 = (bf16[8,96,256]{2,1,0:T(8,128)(2,1)S(1)}, bf16[8,96,256]{2,1,0:T(8,128)(2,1)}, u32[]{:S(2)}) copy-start(bf16[8,96,256]{2,1,0:T(8,128)(2,1)} %basis_ref.3) | copy-start | bytes 1179652
  63.7 21.8 %copy-start.24 = (s32[12]{0:T(128)S(1)}, s32[12]{0:T(128)}, u32[]{:S(2)}) copy-start(s32[12]{0:T(128)} %ranks_ref.5) | copy-start | bytes 148
  69.8 15.6 %all-to-all-start.2 = ((bf16[8,9,32,128]{3,2,1,0:T(8,128)(2,1)}), bf16[8,9,32,128]{3,2,1,0:T(8,128)(2,1)}, u32[]{:S(2)}, u32[]{:S(2)}) async-start(bf16[8,9,32,128]{3,2,1,0:T(8,128)(2,1)} %add_convert_fusion.3), calls=%async_computation.2 | async-start | bytes 1179648 | tf_op jit(solution)/shard_map/all_to_all | solution.py:208
  75.8 9.6 %collective-permute-start.7 = (bf16[9,32,128]{2,1,0:T(8,128)(2,1)}, bf16[9,32,128]{2,1,0:T(8,128)(2,1)}, u32[]{:S(2)}, u32[]{:S(2)}) collective-permute-start(bf16[9,32,128]{2,1,0:T(8,128)(2,1)} %shard_map.100), channel_id=1, source_target_pairs={{0,16},{1,17},{2,18},{3,19},{4,20},{5,21},{6,22},{7,23},{8,24},{9,... | collective-permute-start | bytes 221192 | tf_op jit(solution)/shard_map/ppermute | solution.py:213
  85.4 0.9 copy-start.6
  86.4 0.9 copy-start.11
  87.3 0.8 copy-start.20
  91.4 0.8 copy-start.12
  92.2 14.1 %all-to-all-start.5 = ((bf16[8,9,32,128]{3,2,1,0:T(8,128)(2,1)}), bf16[8,9,32,128]{3,2,1,0:T(8,128)(2,1)}, u32[]{:S(2)}, u32[]{:S(2)}) async-start(bf16[8,9,32,128]{3,2,1,0:T(8,128)(2,1)} %copy-done.12), calls=%async_computation.5 | async-start | bytes 1179648 | tf_op jit(solution)/shard_map/all_to_all | solution.py:208
  97.4 5.9 %collective-permute-start.8 = (bf16[9,32,128]{2,1,0:T(8,128)(2,1)S(1)}, bf16[9,32,128]{2,1,0:T(8,128)(2,1)S(1)}, u32[]{:S(2)}, u32[]{:S(2)}) collective-permute-start(bf16[9,32,128]{2,1,0:T(8,128)(2,1)S(1)} %slice_bitcast_fusion.1), channel_id=1, source_target_pairs={{0,16},{1,17},{2,18},{3,19},{4,20},{5,21},{6,22},{7,23},{8,24},{9,... | collective-permute-start | bytes 221192 | tf_op jit(solution)/shard_map/ppermute | solution.py:213
  103.4 0.9 copy-start.4
  106.3 14.1 %all-to-all-start.4 = ((bf16[8,9,32,128]{3,2,1,0:T(8,128)(2,1)}), bf16[8,9,32,128]{3,2,1,0:T(8,128)(2,1)}, u32[]{:S(2)}, u32[]{:S(2)}) async-start(bf16[8,9,32,128]{3,2,1,0:T(8,128)(2,1)} %copy-done.4), calls=%async_computation.4 | async-start | bytes 1179648 | tf_op jit(solution)/shard_map/all_to_all | solution.py:208
  111.4 6.6 %collective-permute-start.10 = (bf16[1,32,256]{2,1,0:T(8,128)(2,1)S(1)}, bf16[1,32,256]{2,1,0:T(8,128)(2,1)S(1)}, u32[]{:S(2)}, u32[]{:S(2)}) collective-permute-start(bf16[1,32,256]{2,1,0:T(8,128)(2,1)S(1)} %get-tuple-element.34), channel_id=1, source_target_pairs={{1,0},{2,1},{3,2},{4,3},{5,4},{6,5},{7,6},{8,7},{9,8},{10,9},{11,1... | collective-permute-start | bytes 49160 | tf_op jit(solution)/shard_map/ppermute | solution.py:307
  112.7 5.3 %collective-permute-start.9 = (bf16[1,32,256]{2,1,0:T(8,128)(2,1)S(1)}, bf16[1,32,256]{2,1,0:T(8,128)(2,1)S(1)}, u32[]{:S(2)}, u32[]{:S(2)}) collective-permute-start(bf16[1,32,256]{2,1,0:T(8,128)(2,1)S(1)} %get-tuple-element.35), channel_id=1, source_target_pairs={{0,1},{1,2},{2,3},{3,4},{4,5},{5,6},{6,7},{7,8},{8,9},{9,10},{10,1... | collective-permute-start | bytes 49160 | tf_op jit(solution)/shard_map/ppermute | solution.py:306
  115.8 0.9 copy-start.23
  117.3 0.7 copy-start.8
  118.1 0.6 copy-start.21
  118.8 3.5 %collective-permute-start.11 = (bf16[8,9,32,128]{3,2,1,0:T(8,128)(2,1)}, bf16[8,9,32,128]{3,2,1,0:T(8,128)(2,1)S(1)}, u32[]{:S(2)}, u32[]{:S(2)}) collective-permute-start(bf16[8,9,32,128]{3,2,1,0:T(8,128)(2,1)} %all-to-all-done.5.refs_0_), channel_id=1, source_target_pairs={{0,1},{1,0},{2,3},{3,2},{4,5},{5,4},{6,7},{7,6},{8,9},{9,8},{10,11... | collective-permute-start | bytes 1769480 | tf_op jit(solution)/shard_map/ppermute | solution.py:216
  120.4 2.7 %collective-permute-start.12 = (bf16[8,9,32,128]{3,2,1,0:T(8,128)(2,1)}, bf16[8,9,32,128]{3,2,1,0:T(8,128)(2,1)S(1)}, u32[]{:S(2)}, u32[]{:S(2)}) collective-permute-start(bf16[8,9,32,128]{3,2,1,0:T(8,128)(2,1)} %all-to-all-done.4.refs_1_), channel_id=1, source_target_pairs={{0,1},{1,0},{2,3},{3,2},{4,5},{5,4},{6,7},{7,6},{8,9},{9,8},{10,11... | collective-permute-start | bytes 1769480 | tf_op jit(solution)/shard_map/ppermute | solution.py:216
  122.3 0.9 copy-start.14
  123.1 1.9 %copy-start.2 = (bf16[128,96,96]{2,1,0:T(8,128)(2,1)S(1)}, bf16[128,96,96]{2,1,0:T(8,128)(2,1)}, u32[]{:S(2)}) copy-start(bf16[128,96,96]{2,1,0:T(8,128)(2,1)} %copy.10.coupling_ref) | copy-start | bytes 7077892
  125.0 1.1 copy-start.15
  133.1 0.8 copy-start.16
  133.9 2.0 %collective-permute-start.14 = (bf16[8,9,32,128]{3,2,1,0:T(8,128)(2,1)S(1)}, bf16[8,9,32,128]{3,2,1,0:T(8,128)(2,1)S(1)}, u32[]{:S(2)}, u32[]{:S(2)}) collective-permute-start(bf16[8,9,32,128]{3,2,1,0:T(8,128)(2,1)S(1)} %get-tuple-element.33), channel_id=1, source_target_pairs={{0,1},{1,0},{2,3},{3,2},{4,5},{5,4},{6,7},{7,6},{8,9},{9,8},{10,11... | collective-permute-start | bytes 1769480 | tf_op jit(solution)/shard_map/ppermute | solution.py:216
  135.9 7.5 %copy-start.17 = (bf16[8,9,32,128]{3,2,1,0:T(8,128)(2,1)S(1)}, bf16[8,9,32,128]{3,2,1,0:T(8,128)(2,1)}, u32[]{:S(2)}) copy-start(bf16[8,9,32,128]{3,2,1,0:T(8,128)(2,1)} %copy-done.16) | copy-start | bytes 1769476
  136.9 14.7 %all-to-all-start.7 = ((bf16[8,9,32,128]{3,2,1,0:T(8,128)(2,1)}), bf16[8,9,32,128]{3,2,1,0:T(8,128)(2,1)S(1)}, u32[]{:S(2)}, u32[]{:S(2)}) async-start(bf16[8,9,32,128]{3,2,1,0:T(8,128)(2,1)} %add_convert_fusion), calls=%async_computation.7 | async-start | bytes 1179648 | tf_op jit(solution)/shard_map/all_to_all | solution.py:208
  141.3 2.0 %collective-permute-start.13 = (bf16[8,9,32,128]{3,2,1,0:T(8,128)(2,1)S(1)}, bf16[8,9,32,128]{3,2,1,0:T(8,128)(2,1)S(1)}, u32[]{:S(2)}, u32[]{:S(2)}) collective-permute-start(bf16[8,9,32,128]{3,2,1,0:T(8,128)(2,1)S(1)} %get-tuple-element.31), channel_id=1, source_target_pairs={{0,1},{1,0},{2,3},{3,2},{4,5},{5,4},{6,7},{7,6},{8,9},{9,8},{10,11... | collective-permute-start | bytes 1769480 | tf_op jit(solution)/shard_map/ppermute | solution.py:216
  144.3 21.5 %copy-start.7 = (bf16[8,96,96]{2,1,0:T(8,128)(2,1)S(1)}, bf16[8,96,96]{2,1,0:T(8,128)(2,1)}, u32[]{:S(2)}) copy-start(bf16[8,96,96]{2,1,0:T(8,128)(2,1)} %transfer_ref.3) | copy-start | bytes 442372
  144.3 21.5 %copy-start.9 = (f32[8,32,256]{2,1,0:T(8,128)S(1)}, f32[8,32,256]{2,1,0:T(8,128)}, u32[]{:S(2)}) copy-start(f32[8,32,256]{2,1,0:T(8,128)} %copy-done.8) | copy-start | bytes 786436
  144.3 21.5 %copy-start.22 = (f32[2,32,256]{2,1,0:T(8,128)S(1)}, f32[2,32,256]{2,1,0:T(8,128)}, u32[]{:S(2)}) copy-start(f32[2,32,256]{2,1,0:T(8,128)} %copy-done.21) | copy-start | bytes 196612
  151.5 14.3 %all-to-all-start.6 = ((bf16[8,9,32,128]{3,2,1,0:T(8,128)(2,1)}), bf16[8,9,32,128]{3,2,1,0:T(8,128)(2,1)S(1)}, u32[]{:S(2)}, u32[]{:S(2)}) async-start(bf16[8,9,32,128]{3,2,1,0:T(8,128)(2,1)} %add_convert_fusion.1), calls=%async_computation.6 | async-start | bytes 1179648 | tf_op jit(solution)/shard_map/all_to_all | solution.py:208
  155.2 10.7 %collective-permute-start.15 = (bf16[9,32,128]{2,1,0:T(8,128)(2,1)S(1)}, bf16[9,32,128]{2,1,0:T(8,128)(2,1)S(1)}, u32[]{:S(2)}, u32[]{:S(2)}) collective-permute-start(bf16[9,32,128]{2,1,0:T(8,128)(2,1)S(1)} %shard_map.106), channel_id=1, source_target_pairs={{0,16},{1,17},{2,18},{3,19},{4,20},{5,21},{6,22},{7,23},{8,24},{9,... | collective-permute-start | bytes 221192 | tf_op jit(solution)/shard_map/ppermute | solution.py:213

commit v5 on v4

--- a/solution.py
+++ b/solution.py
@@ -47,7 +47,7 @@
 
 
 def emit_coeffs(read_leaf, basis_ref, transfer_ref, ranks_ref, out_ref, leaves, rank_top):
-    copies, mains, rhs, _ = out_ref.shape
+    mains, rhs, _ = out_ref.shape
     lane = lax.broadcasted_iota(jnp.int32, (rhs, rank_top), 1)
     coeffs = []
     for i in range(leaves):
@@ -59,9 +59,7 @@
     wide = [widen(value.astype(F32)) for value in coeffs]
     for q in range(mains // 3):
         for k, tile in enumerate(packed(wide[3 * q : 3 * q + 3], wide[mains + q], rank_top)):
-            tile = tile.astype(BF)
-            for c in range(copies):
-                out_ref[c, 3 * q + k] = tile
+            out_ref[3 * q + k] = tile.astype(BF)
 
 
 def fetch(pairs, sems):
@@ -78,17 +76,18 @@
     emit_coeffs(lambda i: v_ref[i], basis_ref, transfer_ref, ranks_ref, out_ref, leaves, rank_top)
 
 
-def couple_kernel(source_ref, target_ref, coupling_ref, *refs, sets, unroll):
-    in_refs, out_refs, (sources, total) = refs[:sets], refs[sets : 2 * sets], refs[2 * sets :]
+def couple_kernel(source_ref, target_ref, coupling_ref, *refs, order, unroll):
+    chips = sum(len(group) for group in order)
+    in_refs, out_refs, (sources, total) = refs[: 2 * chips], refs[2 * chips : -2], refs[-2:]
     blocks, rank_top, _ = coupling_ref.shape
-    chips, mains, rhs, _ = in_refs[0].shape
+    far, mains, rhs, _ = in_refs[0].shape
     quads = mains // 3
     clusters = mains + quads
 
-    def split(d, _):
+    def split(f, _):
         for n, packed_ref in enumerate(in_refs):
-            row = (n * chips + d) * clusters
-            tiles = [packed_ref[d, c] for c in range(mains)]
+            row = (n * far + f) * clusters
+            tiles = [packed_ref[f, c] for c in range(mains)]
             for c in range(mains):
                 sources[row + c] = tiles[c]
             for q in range(quads):
@@ -98,7 +97,7 @@
                 total[row + c] = jnp.zeros((rhs, LANES), F32)
         return 0
 
-    lax.fori_loop(0, chips, split, 0)
+    lax.fori_loop(0, far, split, 0)
 
     def some(s, _):
         for u in range(unroll):
@@ -110,16 +109,18 @@
 
     lax.fori_loop(0, blocks // unroll, some, 0)
 
-    def pack(d, _):
-        for n, packed_ref in enumerate(out_refs):
-            row = (n * chips + d) * clusters
-            for q in range(quads):
-                mains_now = [total[row + 3 * q + k] for k in range(3)]
-                for k, tile in enumerate(packed(mains_now, total[row + mains + q], rank_top)):
-                    packed_ref[d, 3 * q + k] = tile.astype(BF)
+    def pack(f, _):
+        for core in range(2):
+            for g, group in enumerate(order):
+                for place, chip in enumerate(group):
+                    row = ((core * chips + chip) * far + f) * clusters
+                    for q in range(quads):
+                        mains_now = [total[row + 3 * q + k] for k in range(3)]
+                        for k, tile in enumerate(packed(mains_now, total[row + mains + q], rank_top)):
+                            out_refs[core * len(order) + g][place, f, 3 * q + k] = tile.astype(BF)
         return 0
 
-    lax.fori_loop(0, chips, pack, 0)
+    lax.fori_loop(0, far, pack, 0)
 
 
 def near_kernel(v_ref, near_ref, out_ref):
@@ -138,32 +139,39 @@
     out_ref[1] = dot(after_ref[0], last_ref[0, 0])
 
 
-def part_sum(parts_ref, t):
-    tile = parts_ref[0, t].astype(F32)
-    for p in range(1, parts_ref.shape[0]):
-        tile = tile + parts_ref[p, t].astype(F32)
-    return tile
-
-
-def sum_kernel(parts_ref, out_ref):
-    for t in range(out_ref.shape[0]):
-        out_ref[t] = part_sum(parts_ref, t).astype(BF)
-
-
-def copy_kernel(in_ref, out_ref):
-    for t in range(in_ref.shape[0]):
-        tile = in_ref[t]
-        for c in range(out_ref.shape[0]):
-            out_ref[c, t] = tile
-
-
-def field_kernel(ranks_ref, near_ref, edge_ref, basis_ref, transfer_ref, parts_ref, *rest, away):
+def first_add_kernel(keep_ref, swap_ref, *out_refs):
+    for n, out_ref in enumerate(out_refs):
+        out_ref[...] = (keep_ref[n].astype(F32) + swap_ref[n].astype(F32)).astype(BF)
+
+
+def second_add_kernel(keep_ref, swap_ref, y_ref, z_ref, own_out, y_out, z_out):
+    own_out[...] = keep_ref[0].astype(F32) + swap_ref[0].astype(F32)
+    for n, part_ref, out_ref in ((2, y_ref, y_out), (3, z_ref, z_out)):
+        total = keep_ref[n].astype(F32) + swap_ref[n].astype(F32) + part_ref[...].astype(F32)
+        out_ref[...] = total.astype(BF)
+
+
+def third_add_kernel(keep_ref, swap_ref, x_ref, x_out):
+    total = keep_ref[1].astype(F32) + swap_ref[1].astype(F32) + x_ref[...].astype(F32)
+    x_out[...] = total.astype(BF)
+
+
+def last_add_kernel(own_ref, x_ref, y_ref, z_ref, keep_out, *away_refs):
+    for f in range(own_ref.shape[0]):
+        total = own_ref[f] + x_ref[f].astype(F32) + y_ref[f].astype(F32) + z_ref[f].astype(F32)
+        if f == 0:
+            keep_out[...] = total
+        else:
+            away_refs[f - 1][...] = total.astype(BF)
+
+
+def field_kernel(ranks_ref, near_ref, edge_ref, basis_ref, transfer_ref, keep_ref, *rest, away):
     term_refs, out_ref, coeff_ref = rest[:away], rest[away], rest[away + 1 :]
     leaves, rank_top, _ = basis_ref.shape
-    _, mains, rhs, _ = parts_ref.shape
+    mains, rhs, _ = keep_ref.shape
     tiles = []
     for t in range(mains):
-        tile = part_sum(parts_ref, t)
+        tile = keep_ref[t]
         for term_ref in term_refs:
             tile = tile + term_ref[t].astype(F32)
         tiles.append(tile)
@@ -201,17 +209,14 @@
     cores, chips = 2, 8
     cube = cores * chips
     far = devices // cube
-    half = chips * far
-    cube_groups = [[f * cube + q * cores + k for q in range(chips)] for f in range(far) for k in range(cores)]
-
-    def exchange(parts):
-        return lax.all_to_all(
-            parts, "clu", split_axis=0, concat_axis=0, tiled=True, axis_index_groups=cube_groups
-        )
+    x, y, z = 1, 2, 4
 
     def swap_far(part, shift):
         return lax.ppermute(part, "clu", [(d, (d + shift * cube) % devices) for d in range(devices)])
 
+    def swap(part, chip):
+        return lax.ppermute(part, "clu", [(d, d ^ chip * cores) for d in range(devices)])
+
     def swap_cores(part):
         return lax.ppermute(part, "clu", [(d, d ^ 1) for d in range(devices)])
 
@@ -219,19 +224,20 @@
 
     def rows(cluster, sign):
         device = cluster // clusters
-        core = (device + me) % cores
-        chip = (device // cores) % chips
+        core = (device ^ me) % cores
+        chip = ((device ^ me) // cores) % chips
         away = (sign * (device // cube - me // cube)) % far
-        return ((core * far + away) * chips + chip) * clusters + cluster % clusters
+        return ((core * chips + chip) * far + away) * clusters + cluster % clusters
 
     source_rows, target_rows = rows(block_source, -1), rows(block_target, 1)
 
     tile_shape = (mains, rhs, LANES)
     out_shape = shape((leaves, rhs, width), BF)
-    part_shape = shape((chips,) + tile_shape, BF)
+    tile_out = shape(tile_shape, BF)
+    part_shape = shape((far,) + tile_shape, BF)
     first_coeffs = pl.pallas_call(
         coeff_kernel,
-        out_shape=part_shape,
+        out_shape=tile_out,
         in_specs=[SMEM, HBM, HBM, HBM],
         out_specs=VMEM,
         scratch_shapes=[
@@ -242,12 +248,12 @@
         ],
     )(ranks, charges, basis, transfer)
 
-    sets = cores * far
+    order = ((x | y | z, x | y, y | z, z | x), (0, x, y, z))
     couple = pl.pallas_call(
-        functools.partial(couple_kernel, sets=sets, unroll=8),
-        out_shape=[part_shape] * sets,
-        in_specs=[SMEM, SMEM, VMEM] + [VMEM] * sets,
-        out_specs=[VMEM] * sets,
+        functools.partial(couple_kernel, order=order, unroll=8),
+        out_shape=[shape((4, far) + tile_shape, BF)] * 4,
+        in_specs=[SMEM, SMEM, VMEM] + [VMEM] * (cores * chips),
+        out_specs=[VMEM] * 4,
         scratch_shapes=[
             pltpu.VMEM((devices * clusters, rhs, LANES), BF),
             pltpu.VMEM((devices * clusters, rhs, LANES), F32),
@@ -283,17 +289,25 @@
         compiler_params=params(16),
     )
 
-    add_parts = pl.pallas_call(
-        sum_kernel, out_shape=shape(tile_shape, BF), in_specs=[VMEM], out_specs=VMEM, compiler_params=params(16)
-    )
-    copies = pl.pallas_call(
-        copy_kernel, out_shape=part_shape, in_specs=[VMEM], out_specs=VMEM, compiler_params=params(16)
-    )
+    def adder(kernel, inputs, outputs):
+        return pl.pallas_call(
+            kernel,
+            out_shape=outputs,
+            in_specs=[VMEM] * inputs,
+            out_specs=[VMEM] * len(outputs),
+            compiler_params=params(16),
+        )
+
+    own_shape = shape((far,) + tile_shape, F32)
+    first_add = adder(first_add_kernel, 2, [part_shape] * 4)
+    second_add = adder(second_add_kernel, 4, [own_shape, part_shape, part_shape])
+    third_add = adder(third_add_kernel, 3, [part_shape])
+    last_add = adder(last_add_kernel, 4, [shape(tile_shape, F32)] + [tile_out] * (far - 1))
 
     def finish(with_coeffs):
         return pl.pallas_call(
             functools.partial(field_kernel, away=far - 1),
-            out_shape=[out_shape, part_shape] if with_coeffs else [out_shape],
+            out_shape=[out_shape, tile_out] if with_coeffs else [out_shape],
             in_specs=[SMEM] + [VMEM] * (4 + far),
             out_specs=[VMEM, VMEM] if with_coeffs else [VMEM],
             compiler_params=params(16),
@@ -302,23 +316,28 @@
     ends = devices - 1
 
     def apply_matrix(field_in, coeffs, with_coeffs):
-        away = [swap_far(coeffs[0], s) for s in range(1, far)]
+        got = {0: jnp.stack([coeffs] + [swap_far(coeffs, s) for s in range(1, far)])}
+        got[x], got[y], got[z] = lax.optimization_barrier((swap(got[0], x), swap(got[0], y), swap(got[0], z)))
+        got[x | y], got[y | z], got[z | x] = swap(got[x], y), swap(got[y], z), swap(got[z], x)
+        got[x | y | z] = swap(got[x | y], z)
         before = lax.ppermute(field_in[leaves - 1 :], "clu", [(i, i + 1) for i in range(ends)])
         after = lax.ppermute(field_in[:1], "clu", [(i + 1, i) for i in range(ends)])
-        own = [exchange(coeffs)]
-        own += [exchange(copies(part)) for part in away]
         near_sum = near(field_in, near_field)
         edges = edge(before, after, near_field, near_field)
-        own[-1], near_sum, edges = lax.optimization_barrier((own[-1], near_sum, edges))
+        got[7], near_sum, edges = lax.optimization_barrier((got[7], near_sum, edges))
+        own = [got[chip] for chip in range(chips)]
         other = [swap_cores(part) for part in own]
-        totals = couple(source_rows, target_rows, coupling, *own, *other)
-        terms = []
-        for s in list(range(1, far)) + [0]:
-            chip_sum = totals[s].astype(F32) + swap_cores(totals[far + s]).astype(F32)
-            parts = exchange(chip_sum.astype(BF))
-            if s:
-                terms.append(swap_far(add_parts(parts), s))
-        return finish(with_coeffs)(ranks, near_sum, edges, basis, transfer, parts, *terms)
+        keep_first, keep, send_first, send = couple(source_rows, target_rows, coupling, *own, *other)
+        far_corner, xy, yz, zx = first_add(keep_first, swap_cores(send_first))
+        swapped = swap_cores(send)
+        yz, zx = swap(yz, z), swap(zx, x)
+        xy = (xy.astype(F32) + swap(far_corner, z).astype(F32)).astype(BF)
+        xy = swap(xy, y)
+        mine, to_y, to_z = second_add(keep, swapped, yz, zx)
+        (to_x,) = third_add(keep, swapped, xy)
+        total, *away = last_add(mine, swap(to_x, x), swap(to_y, y), swap(to_z, z))
+        terms = [swap_far(part, s + 1) for s, part in enumerate(away)]
+        return finish(with_coeffs)(ranks, near_sum, edges, basis, transfer, total, *terms)
 
     first, second_coeffs = apply_matrix(charges, first_coeffs, True)
     (second,) = apply_matrix(first, second_coeffs, False)

time: 170 us -> 148 us (0.87)
  local copies, waits for them, and re-layouts: 24.4 us -> 8.03 us
  waiting for transfers between devices: 49.9 us -> 57.9 us
  Pallas kernels: 26.7 us -> 21.7 us
  other arithmetic: 5.05 us -> 1.05 us
  starting transfers between devices: 61.4 us -> 58.1 us
    ppermute x0 -> x28, waiting for transfers between devices: none -> 39 us  [swap(): lax.ppermute(part, 'clu', [(d, d ^ chip * cores) for d in range(devices)])]
    all_to_all x8 -> x0, starting transfers between devices: 37.6 us -> none  [exchange(): lax.all_to_all(parts, 'clu', split_axis=0, concat_axis=0, tiled=True, axi...]
    ppermute x0 -> x28, starting transfers between devices: none -> 32.7 us  [swap(): lax.ppermute(part, 'clu', [(d, d ^ chip * cores) for d in range(devices)])]
    all_to_all x8 -> x0, waiting for transfers between devices: 31.9 us -> none  [exchange(): lax.all_to_all(parts, 'clu', split_axis=0, concat_axis=0, tiled=True, axi...]
    unnamed x57 -> x27, local copies, waits for them, and re-layouts: 21.8 us -> 6.56 us
    pallas_call x9 -> x13, Pallas kernels: 25.2 us -> 20.2 us  [the longest x2 11.5 us: apply_matrix(): couple(source_rows, target_rows, coupling, *own, *other)]
    convert_element_type x4 -> x2, other arithmetic: 5.01 us -> 0.09 us  [apply_matrix(): xy = (xy.astype(F32) + swap(far_corner, z).astype(F32)).astype(BF)]
    ppermute x4, waiting for transfers between devices: 8.81 us -> 13.5 us  [swap_far(): lax.ppermute(part, 'clu', [(d, (d + shift * cube) % devices) for d in ran...]
  transfers between devices with their start and end apart: 24 -> 56, of which waited for: 13 -> 35; matrix products, arithmetic and copies ran while one was open for 6% -> 4% of each run, Pallas kernels for 2% -> 1%
where the time goes in v5:
time: 148 us
  starting transfers between devices  58.1 us (39%)
  waiting for transfers between devices  57.9 us (39%)
  Pallas kernels  21.7 us (15%)
  local copies, waits for them, and re-layouts  8.03 us (5%)
    ppermute x28, waiting for transfers between devices, swap(): lax.ppermute(part, 'clu', [(d, d ^ chip * cores) for d in range(devices)])  39 us
    ppermute x28, starting transfers between devices, swap(): lax.ppermute(part, 'clu', [(d, d ^ chip * cores) for d in range(devices)])  32.7 us
    ppermute x4, waiting for transfers between devices, swap_far(): lax.ppermute(part, 'clu', [(d, (d + shift * cube) % devices) for d in ran...  13.5 us
    pallas_call x2, Pallas kernels, apply_matrix(): couple(source_rows, target_rows, coupling, *own, *other)  11.5 us
    ppermute x4, starting transfers between devices, swap_far(): lax.ppermute(part, 'clu', [(d, (d + shift * cube) % devices) for d in ran...  10.7 us
    unnamed x27, local copies, waits for them, and re-layouts  6.56 us
    ppermute x20, starting transfers between devices, swap_cores(): return lax.ppermute(part, 'clu', [(d, d ^ 1) for d in range(devices)])  6.08 us
    ppermute x2, starting transfers between devices, apply_matrix(): lax.ppermute(field_in[leaves - 1:], 'clu', [(i, i + 1) for i in range(end...  6.06 us
  transfers between devices with their start and end apart: 56, of which 35 were waited for; matrix products, arithmetic and copies ran while one was open for 4% of the time, Pallas kernels for 1%

profile of v5, /device:TPU:0, one launch (start us, length us, event | category | flops | bytes accessed | tf_op | source)
XLA Modules:
  0.0 147.6 jit_solution(17585094973912790368)
XLA Ops:
  0.6 2.9 %shard_map.95 = bf16[9,32,128]{2,1,0:T(8,128)(2,1)} custom-call(s32[12]{0:T(128)} %ranks_ref.5, bf16[8,32,256]{2,1,0:T(8,128)(2,1)} %v_ref.1, bf16[8,96,256]{2,1,0:T(8,128)(2,1)} %basis_ref.3, bf16[8,96,96]{2,1,0:T(8,128)(2,1)} %transfer_ref.3), custom_call_target="tpu_custom_call" | custom-call | tf_op jit(solution)/shard_map/pallas_call | solution.py:238
  3.6 4.1 %collective-permute-start = (bf16[9,32,128]{2,1,0:T(8,128)(2,1)}, bf16[9,32,128]{2,1,0:T(8,128)(2,1)S(1)}, u32[]{:S(2)}, u32[]{:S(2)}) collective-permute-start(bf16[9,32,128]{2,1,0:T(8,128)(2,1)} %shard_map.95), channel_id=1, source_target_pairs={{0,16},{1,17},{2,18},{3,19},{4,20},{5,21},{6,22},{7,23},{8,24},{9,... | collective-permute-start | bytes 221192 | tf_op jit(solution)/shard_map/ppermute | solution.py:215
  7.7 4.1 %collective-permute-done = bf16[9,32,128]{2,1,0:T(8,128)(2,1)S(1)} collective-permute-done((bf16[9,32,128]{2,1,0:T(8,128)(2,1)}, bf16[9,32,128]{2,1,0:T(8,128)(2,1)S(1)}, u32[]{:S(2)}, u32[]{:S(2)}) %collective-permute-start) | collective-permute-done | bytes 73760 | tf_op jit(solution)/shard_map/ppermute | solution.py:215
  11.8 0.9 pad_maximum_fusion.refs_0_
  12.7 0.8 collective-permute-start.3
  13.5 1.5 %collective-permute-start.2 = (bf16[2,9,32,128]{3,2,1,0:T(8,128)(2,1)S(1)}, bf16[2,9,32,128]{3,2,1,0:T(8,128)(2,1)}, u32[]{:S(2)}, u32[]{:S(2)}) collective-permute-start(bf16[2,9,32,128]{3,2,1,0:T(8,128)(2,1)S(1)} %pad_maximum_fusion.refs_0_), channel_id=1, source_target_pairs={{0,4},{1,5},{2,6},{3,7},{4,0},{5,1},{6,2},{7,3},{8,12},{9,13},{10,... | collective-permute-start | bytes 442376 | tf_op jit(solution)/shard_map/ppermute | solution.py:218
  15.0 1.5 %collective-permute-start.1 = (bf16[2,9,32,128]{3,2,1,0:T(8,128)(2,1)S(1)}, bf16[2,9,32,128]{3,2,1,0:T(8,128)(2,1)}, u32[]{:S(2)}, u32[]{:S(2)}) collective-permute-start(bf16[2,9,32,128]{3,2,1,0:T(8,128)(2,1)S(1)} %pad_maximum_fusion.refs_0_), channel_id=1, source_target_pairs={{0,2},{1,3},{2,0},{3,1},{4,6},{5,7},{6,4},{7,5},{8,10},{9,11},{10,... | collective-permute-start | bytes 442376 | tf_op jit(solution)/shard_map/ppermute | solution.py:218
  16.5 1.5 collective-permute-done.3.refs_4_
  18.0 0.9 collective-permute-done.2.refs_2_
  18.9 1.4 collective-permute-done.1.refs_1_
  20.8 4.8 %collective-permute-done.4.refs_3_ = bf16[2,9,32,128]{3,2,1,0:T(8,128)(2,1)S(1)} collective-permute-done((bf16[2,9,32,128]{3,2,1,0:T(8,128)(2,1)}, bf16[2,9,32,128]{3,2,1,0:T(8,128)(2,1)S(1)}, u32[]{:S(2)}, u32[]{:S(2)}) %collective-permute-start.4) | collective-permute-done | bytes 147488 | tf_op jit(solution)/shard_map/ppermute | solution.py:218
  25.6 1.5 collective-permute-start.5
  27.8 1.3 collective-permute-start.7
  29.1 3.0 %collective-permute-start.6 = (bf16[1,32,256]{2,1,0:T(8,128)(2,1)S(1)}, bf16[1,32,256]{2,1,0:T(8,128)(2,1)S(1)}, u32[]{:S(2)}, u32[]{:S(2)}) collective-permute-start(bf16[1,32,256]{2,1,0:T(8,128)(2,1)S(1)} %get-tuple-element.85), channel_id=1, source_target_pairs={{0,1},{1,2},{2,3},{3,4},{4,5},{5,6},{6,7},{7,8},{8,9},{9,10},{10,1... | collective-permute-start | bytes 49160 | tf_op jit(solution)/shard_map/ppermute | solution.py:323
  32.2 1.2 collective-permute-start.10
  34.0 2.3 %collective-permute-start.8 = (bf16[2,9,32,128]{3,2,1,0:T(8,128)(2,1)}, bf16[2,9,32,128]{3,2,1,0:T(8,128)(2,1)}, u32[]{:S(2)}, u32[]{:S(2)}) collective-permute-start(bf16[2,9,32,128]{3,2,1,0:T(8,128)(2,1)} %collective-permute-done.3.refs_4_), channel_id=1, source_target_pairs={{0,2},{1,3},{2,0},{3,1},{4,6},{5,7},{6,4},{7,5},{8,10},{9,11},{10,... | collective-permute-start | bytes 442376 | tf_op jit(solution)/shard_map/ppermute | solution.py:218
  37.0 4.8 %copy.10.coupling_ref = bf16[128,96,96]{2,1,0:T(8,128)(2,1)} copy(bf16[128,96,96]{0,2,1:T(8,128)(2,1)} %param.12) | data formatting | bytes 4718592 | tf_op args[4]
  45.7 6.2 %shard_map.98 = (bf16[4,2,9,32,128]{4,3,2,1,0:T(8,128)(2,1)S(1)}, bf16[4,2,9,32,128]{4,3,2,1,0:T(8,128)(2,1)S(1)}, bf16[4,2,9,32,128]{4,3,2,1,0:T(8,128)(2,1)S(1)}, bf16[4,2,9,32,128]{4,3,2,1,0:T(8,128)(2,1)S(1)}) custom-call(s32[128]{0:T(128)S(1)} %get-tuple-element.86.source_ref, s32[128]{0:T(128)S(1)} %get-tuple-element.87.target_ref, ...), custom_call_target="tpu_custom_call" | custom-call | flops 75497472 | bytes 10485760 | tf_op jit(solution)/shard_map/pallas_call | solution.py:330
  52.5 1.5 %collective-permute-done.19.swap_ref = bf16[4,2,9,32,128]{4,3,2,1,0:T(8,128)(2,1)S(1)} collective-permute-done((bf16[4,2,9,32,128]{4,3,2,1,0:T(8,128)(2,1)S(1)}, bf16[4,2,9,32,128]{4,3,2,1,0:T(8,128)(2,1)S(1)}, u32[]{:S(2)}, u32[]{:S(2)}) %collective-permute-start.19) | collective-permute-done | bytes 589856 | tf_op jit(solution)/shard_map/ppermute | solution.py:221
  54.1 0.9 collective-permute-start.22
  55.1 1.2 collective-permute-start.20
  56.2 0.9 collective-permute-start.21
  57.2 3.7 %collective-permute-done.22 = bf16[2,9,32,128]{3,2,1,0:T(8,128)(2,1)S(1)} collective-permute-done((bf16[2,9,32,128]{3,2,1,0:T(8,128)(2,1)S(1)}, bf16[2,9,32,128]{3,2,1,0:T(8,128)(2,1)S(1)}, u32[]{:S(2)}, u32[]{:S(2)}) %collective-permute-start.22) | collective-permute-done | bytes 147488 | tf_op jit(solution)/shard_map/ppermute | solution.py:218
  60.9 1.2 collective-permute-start.23
  62.1 1.2 collective-permute-done.20.y_ref
  63.5 1.2 collective-permute-start.25
  65.0 1.8 %collective-permute-done.23.x_ref = bf16[2,9,32,128]{3,2,1,0:T(8,128)(2,1)S(1)} collective-permute-done((bf16[2,9,32,128]{3,2,1,0:T(8,128)(2,1)S(1)}, bf16[2,9,32,128]{3,2,1,0:T(8,128)(2,1)S(1)}, u32[]{:S(2)}, u32[]{:S(2)}) %collective-permute-start.23) | collective-permute-done | bytes 147488 | tf_op jit(solution)/shard_map/ppermute | solution.py:218
  67.1 2.2 %collective-permute-done.25.y_ref = bf16[2,9,32,128]{3,2,1,0:T(8,128)(2,1)S(1)} collective-permute-done((bf16[2,9,32,128]{3,2,1,0:T(8,128)(2,1)S(1)}, bf16[2,9,32,128]{3,2,1,0:T(8,128)(2,1)S(1)}, u32[]{:S(2)}, u32[]{:S(2)}) %collective-permute-start.25) | collective-permute-done | bytes 147488 | tf_op jit(solution)/shard_map/ppermute | solution.py:218
  69.8 2.2 %collective-permute-done.24.x_ref = bf16[2,9,32,128]{3,2,1,0:T(8,128)(2,1)S(1)} collective-permute-done((bf16[2,9,32,128]{3,2,1,0:T(8,128)(2,1)S(1)}, bf16[2,9,32,128]{3,2,1,0:T(8,128)(2,1)S(1)}, u32[]{:S(2)}, u32[]{:S(2)}) %collective-permute-start.24) | collective-permute-done | bytes 147488 | tf_op jit(solution)/shard_map/ppermute | solution.py:218
  72.1 2.1 %collective-permute-start.27 = (bf16[9,32,128]{2,1,0:T(8,128)(2,1)S(1)}, bf16[9,32,128]{2,1,0:T(8,128)(2,1)S(1)}, u32[]{:S(2)}, u32[]{:S(2)}) collective-permute-start(bf16[9,32,128]{2,1,0:T(8,128)(2,1)S(1)} %get-tuple-element.60), channel_id=1, source_target_pairs={{0,16},{1,17},{2,18},{3,19},{4,20},{5,21},{6,22},{7,23},{8,24},{9,... | collective-permute-start | bytes 221192 | tf_op jit(solution)/shard_map/ppermute | solution.py:215
  74.2 3.2 %collective-permute-done.27.rest_0_ = bf16[9,32,128]{2,1,0:T(8,128)(2,1)S(1)} collective-permute-done((bf16[9,32,128]{2,1,0:T(8,128)(2,1)S(1)}, bf16[9,32,128]{2,1,0:T(8,128)(2,1)S(1)}, u32[]{:S(2)}, u32[]{:S(2)}) %collective-permute-start.27) | collective-permute-done | bytes 73760 | tf_op jit(solution)/shard_map/ppermute | solution.py:215
  77.4 2.5 %shard_map.103 = (bf16[8,32,256]{2,1,0:T(8,128)(2,1)}, bf16[9,32,128]{2,1,0:T(8,128)(2,1)S(1)}) custom-call(s32[12]{0:T(128)S(1)} %copy-done.10, f32[8,32,256]{2,1,0:T(8,128)S(1)} %shard_map.96.near_ref, f32[2,32,256]{2,1,0:T(8,128)S(1)} %shard_map.97.edge_ref, bf16[8,96,256]{2,1,0:T(8,128)(2,1)S(1)} %copy-done.2, bf16[8,96,96]{2,1,0:T(8,128)(2,1)S(1)} %copy-done.3, ...), custom_call_target="tpu_custom_call" | custom-call | tf_op jit(solution)/shard_map/pallas_call | solution.py:340
  79.9 2.0 %collective-permute-start.28 = (bf16[9,32,128]{2,1,0:T(8,128)(2,1)S(1)}, bf16[9,32,128]{2,1,0:T(8,128)(2,1)S(1)}, u32[]{:S(2)}, u32[]{:S(2)}) collective-permute-start(bf16[9,32,128]{2,1,0:T(8,128)(2,1)S(1)} %get-tuple-element.62), channel_id=1, source_target_pairs={{0,16},{1,17},{2,18},{3,19},{4,20},{5,21},{6,22},{7,23},{8,24},{9,... | collective-permute-start | bytes 221192 | tf_op jit(solution)/shard_map/ppermute | solution.py:215
  82.0 3.3 %collective-permute-done.28 = bf16[9,32,128]{2,1,0:T(8,128)(2,1)S(1)} collective-permute-done((bf16[9,32,128]{2,1,0:T(8,128)(2,1)S(1)}, bf16[9,32,128]{2,1,0:T(8,128)(2,1)S(1)}, u32[]{:S(2)}, u32[]{:S(2)}) %collective-permute-start.28) | collective-permute-done | bytes 73760 | tf_op jit(solution)/shard_map/ppermute | solution.py:215
  85.3 2.1 %collective-permute-start.31 = (bf16[2,9,32,128]{3,2,1,0:T(8,128)(2,1)S(1)}, bf16[2,9,32,128]{3,2,1,0:T(8,128)(2,1)S(1)}, u32[]{:S(2)}, u32[]{:S(2)}) collective-permute-start(bf16[2,9,32,128]{3,2,1,0:T(8,128)(2,1)S(1)} %pad_maximum_fusion.1.refs_0_), channel_id=1, source_target_pairs={{0,8},{1,9},{2,10},{3,11},{4,12},{5,13},{6,14},{7,15},{8,0},{9,1},... | collective-permute-start | bytes 442376 | tf_op jit(solution)/shard_map/ppermute | solution.py:218
  87.4 0.9 collective-permute-start.30
  88.3 1.3 collective-permute-start.29
  89.6 1.0 collective-permute-done.31.refs_4_
  90.5 2.0 %collective-permute-done.30.refs_2_ = bf16[2,9,32,128]{3,2,1,0:T(8,128)(2,1)S(1)} collective-permute-done((bf16[2,9,32,128]{3,2,1,0:T(8,128)(2,1)S(1)}, bf16[2,9,32,128]{3,2,1,0:T(8,128)(2,1)S(1)}, u32[]{:S(2)}, u32[]{:S(2)}) %collective-permute-start.30) | collective-permute-done | bytes 147488 | tf_op jit(solution)/shard_map/ppermute | solution.py:218
  92.6 0.9 collective-permute-done.29.refs_1_
  93.4 1.2 collective-permute-start.32
  94.6 4.0 %collective-permute-done.32.refs_3_ = bf16[2,9,32,128]{3,2,1,0:T(8,128)(2,1)S(1)} collective-permute-done((bf16[2,9,32,128]{3,2,1,0:T(8,128)(2,1)S(1)}, bf16[2,9,32,128]{3,2,1,0:T(8,128)(2,1)S(1)}, u32[]{:S(2)}, u32[]{:S(2)}) %collective-permute-start.32) | collective-permute-done | bytes 147488 | tf_op jit(solution)/shard_map/ppermute | solution.py:218
  98.5 1.6 %collective-permute-start.33 = (bf16[2,9,32,128]{3,2,1,0:T(8,128)(2,1)S(1)}, bf16[2,9,32,128]{3,2,1,0:T(8,128)(2,1)S(1)}, u32[]{:S(2)}, u32[]{:S(2)}) collective-permute-start(bf16[2,9,32,128]{3,2,1,0:T(8,128)(2,1)S(1)} %collective-permute-done.32.refs_3_), channel_id=1, source_target_pairs={{0,8},{1,9},{2,10},{3,11},{4,12},{5,13},{6,14},{7,15},{8,0},{9,1},... | collective-permute-start | bytes 442376 | tf_op jit(solution)/shard_map/ppermute | solution.py:218
  100.8 1.3 collective-permute-start.35
  102.1 3.0 %collective-permute-start.34 = (bf16[1,32,256]{2,1,0:T(8,128)(2,1)S(1)}, bf16[1,32,256]{2,1,0:T(8,128)(2,1)S(1)}, u32[]{:S(2)}, u32[]{:S(2)}) collective-permute-start(bf16[1,32,256]{2,1,0:T(8,128)(2,1)S(1)} %get-tuple-element.83), channel_id=1, source_target_pairs={{0,1},{1,2},{2,3},{3,4},{4,5},{5,6},{6,7},{7,8},{8,9},{9,10},{10,1... | collective-permute-start | bytes 49160 | tf_op jit(solution)/shard_map/ppermute | solution.py:323
  105.2 0.8 collective-permute-start.38
  106.7 2.2 %collective-permute-start.36 = (bf16[2,9,32,128]{3,2,1,0:T(8,128)(2,1)S(1)}, bf16[2,9,32,128]{3,2,1,0:T(8,128)(2,1)S(1)}, u32[]{:S(2)}, u32[]{:S(2)}) collective-permute-start(bf16[2,9,32,128]{3,2,1,0:T(8,128)(2,1)S(1)} %collective-permute-done.31.refs_4_), channel_id=1, source_target_pairs={{0,2},{1,3},{2,0},{3,1},{4,6},{5,7},{6,4},{7,5},{8,10},{9,11},{10,... | collective-permute-start | bytes 442376 | tf_op jit(solution)/shard_map/ppermute | solution.py:218
  108.9 0.9 copy-done.5
  111.2 1.0 collective-permute-done.37.refs_6_
  114.2 5.4 %shard_map.106 = (bf16[4,2,9,32,128]{4,3,2,1,0:T(8,128)(2,1)S(1)}, bf16[4,2,9,32,128]{4,3,2,1,0:T(8,128)(2,1)S(1)}, bf16[4,2,9,32,128]{4,3,2,1,0:T(8,128)(2,1)S(1)}, bf16[4,2,9,32,128]{4,3,2,1,0:T(8,128)(2,1)S(1)}) custom-call(s32[128]{0:T(128)S(1)} %get-tuple-element.86.source_ref, s32[128]{0:T(128)S(1)} %get-tuple-element.87.target_ref, ...), custom_call_target="tpu_custom_call" | custom-call | flops 75497472 | bytes 10485760 | tf_op jit(solution)/shard_map/pallas_call | solution.py:330
  120.2 1.5 %collective-permute-done.47.swap_ref = bf16[4,2,9,32,128]{4,3,2,1,0:T(8,128)(2,1)S(1)} collective-permute-done((bf16[4,2,9,32,128]{4,3,2,1,0:T(8,128)(2,1)S(1)}, bf16[4,2,9,32,128]{4,3,2,1,0:T(8,128)(2,1)S(1)}, u32[]{:S(2)}, u32[]{:S(2)}) %collective-permute-start.47) | collective-permute-done | bytes 589856 | tf_op jit(solution)/shard_map/ppermute | solution.py:221
  121.8 2.7 %collective-permute-start.50 = (bf16[2,9,32,128]{3,2,1,0:T(8,128)(2,1)S(1)}, bf16[2,9,32,128]{3,2,1,0:T(8,128)(2,1)S(1)}, u32[]{:S(2)}, u32[]{:S(2)}) collective-permute-start(bf16[2,9,32,128]{3,2,1,0:T(8,128)(2,1)S(1)} %get-tuple-element.77), channel_id=1, source_target_pairs={{0,8},{1,9},{2,10},{3,11},{4,12},{5,13},{6,14},{7,15},{8,0},{9,1},... | collective-permute-start | bytes 442376 | tf_op jit(solution)/shard_map/ppermute | solution.py:218
  124.5 0.8 collective-permute-start.49
  125.3 3.8 %collective-permute-done.50 = bf16[2,9,32,128]{3,2,1,0:T(8,128)(2,1)S(1)} collective-permute-done((bf16[2,9,32,128]{3,2,1,0:T(8,128)(2,1)S(1)}, bf16[2,9,32,128]{3,2,1,0:T(8,128)(2,1)S(1)}, u32[]{:S(2)}, u32[]{:S(2)}) %collective-permute-start.50) | collective-permute-done | bytes 147488 | tf_op jit(solution)/shard_map/ppermute | solution.py:218
  129.1 1.4 collective-permute-start.51
  130.6 1.4 collective-permute-done.48.y_ref
  132.1 1.1 collective-permute-start.53
  133.2 1.0 collective-permute-start.54
  134.5 1.2 collective-permute-start.52
  135.7 2.0 %collective-permute-done.53.y_ref = bf16[2,9,32,128]{3,2,1,0:T(8,128)(2,1)S(1)} collective-permute-done((bf16[2,9,32,128]{3,2,1,0:T(8,128)(2,1)S(1)}, bf16[2,9,32,128]{3,2,1,0:T(8,128)(2,1)S(1)}, u32[]{:S(2)}, u32[]{:S(2)}) %collective-permute-start.53) | collective-permute-done | bytes 147488 | tf_op jit(solution)/shard_map/ppermute | solution.py:218
  138.3 1.4 collective-permute-done.52.x_ref
  139.8 2.5 %collective-permute-start.55 = (bf16[9,32,128]{2,1,0:T(8,128)(2,1)S(1)}, bf16[9,32,128]{2,1,0:T(8,128)(2,1)S(1)}, u32[]{:S(2)}, u32[]{:S(2)}) collective-permute-start(bf16[9,32,128]{2,1,0:T(8,128)(2,1)S(1)} %get-tuple-element.81), channel_id=1, source_target_pairs={{0,16},{1,17},{2,18},{3,19},{4,20},{5,21},{6,22},{7,23},{8,24},{9,... | collective-permute-start | bytes 221192 | tf_op jit(solution)/shard_map/ppermute | solution.py:215
  142.3 2.8 %collective-permute-done.55.rest_0_ = bf16[9,32,128]{2,1,0:T(8,128)(2,1)S(1)} collective-permute-done((bf16[9,32,128]{2,1,0:T(8,128)(2,1)S(1)}, bf16[9,32,128]{2,1,0:T(8,128)(2,1)S(1)}, u32[]{:S(2)}, u32[]{:S(2)}) %collective-permute-start.55) | collective-permute-done | bytes 73760 | tf_op jit(solution)/shard_map/ppermute | solution.py:215
  145.1 2.5 %shard_map.111 = bf16[8,32,256]{2,1,0:T(8,128)(2,1)} custom-call(s32[12]{0:T(128)S(1)} %copy-done.10, f32[8,32,256]{2,1,0:T(8,128)S(1)} %shard_map.104.near_ref, f32[2,32,256]{2,1,0:T(8,128)S(1)} %shard_map.105.edge_ref, bf16[8,96,256]{2,1,0:T(8,128)(2,1)S(1)} %copy-done.2, bf16[8,96,96]{2,1,0:T(8,128)(2,1)S(1)} %copy-done.3, ...), custom_call_target="tpu_custom_call" | custom-call | tf_op jit(solution)/shard_map/pallas_call | solution.py:340
  (99 shorter events, 15.6 us)
Async XLA Ops:
  3.5 38.3 %copy-start = (bf16[8,3,256,256]{3,2,1,0:T(8,128)(2,1)S(1)}, bf16[8,3,256,256]{3,2,1,0:T(8,128)(2,1)}, u32[]{:S(2)}) copy-start(bf16[8,3,256,256]{3,2,1,0:T(8,128)(2,1)} %last_ref.3) | copy-start | bytes 9437188
  3.5 38.2 %copy-start.4 = (bf16[8,32,256]{2,1,0:T(8,128)(2,1)S(1)}, bf16[8,32,256]{2,1,0:T(8,128)(2,1)}, u32[]{:S(2)}) copy-start(bf16[8,32,256]{2,1,0:T(8,128)(2,1)} %v_ref.1) | copy-start | bytes 393220
  3.6 8.2 %collective-permute-start = (bf16[9,32,128]{2,1,0:T(8,128)(2,1)}, bf16[9,32,128]{2,1,0:T(8,128)(2,1)S(1)}, u32[]{:S(2)}, u32[]{:S(2)}) collective-permute-start(bf16[9,32,128]{2,1,0:T(8,128)(2,1)} %shard_map.95), channel_id=1, source_target_pairs={{0,16},{1,17},{2,18},{3,19},{4,20},{5,21},{6,22},{7,23},{8,24},{9,... | collective-permute-start | bytes 221192 | tf_op jit(solution)/shard_map/ppermute | solution.py:215
  12.7 5.3 %collective-permute-start.3 = (bf16[2,9,32,128]{3,2,1,0:T(8,128)(2,1)S(1)}, bf16[2,9,32,128]{3,2,1,0:T(8,128)(2,1)}, u32[]{:S(2)}, u32[]{:S(2)}) collective-permute-start(bf16[2,9,32,128]{3,2,1,0:T(8,128)(2,1)S(1)} %pad_maximum_fusion.refs_0_), channel_id=1, source_target_pairs={{0,8},{1,9},{2,10},{3,11},{4,12},{5,13},{6,14},{7,15},{8,0},{9,1},... | collective-permute-start | bytes 442376 | tf_op jit(solution)/shard_map/ppermute | solution.py:218
  13.5 5.3 %collective-permute-start.2 = (bf16[2,9,32,128]{3,2,1,0:T(8,128)(2,1)S(1)}, bf16[2,9,32,128]{3,2,1,0:T(8,128)(2,1)}, u32[]{:S(2)}, u32[]{:S(2)}) collective-permute-start(bf16[2,9,32,128]{3,2,1,0:T(8,128)(2,1)S(1)} %pad_maximum_fusion.refs_0_), channel_id=1, source_target_pairs={{0,4},{1,5},{2,6},{3,7},{4,0},{5,1},{6,2},{7,3},{8,12},{9,13},{10,... | collective-permute-start | bytes 442376 | tf_op jit(solution)/shard_map/ppermute | solution.py:218
  15.0 5.2 %collective-permute-start.1 = (bf16[2,9,32,128]{3,2,1,0:T(8,128)(2,1)S(1)}, bf16[2,9,32,128]{3,2,1,0:T(8,128)(2,1)}, u32[]{:S(2)}, u32[]{:S(2)}) collective-permute-start(bf16[2,9,32,128]{3,2,1,0:T(8,128)(2,1)S(1)} %pad_maximum_fusion.refs_0_), channel_id=1, source_target_pairs={{0,2},{1,3},{2,0},{3,1},{4,6},{5,7},{6,4},{7,5},{8,10},{9,11},{10,... | collective-permute-start | bytes 442376 | tf_op jit(solution)/shard_map/ppermute | solution.py:218
  20.3 5.4 %collective-permute-start.4 = (bf16[2,9,32,128]{3,2,1,0:T(8,128)(2,1)}, bf16[2,9,32,128]{3,2,1,0:T(8,128)(2,1)S(1)}, u32[]{:S(2)}, u32[]{:S(2)}) collective-permute-start(bf16[2,9,32,128]{3,2,1,0:T(8,128)(2,1)} %collective-permute-done.1.refs_1_), channel_id=1, source_target_pairs={{0,4},{1,5},{2,6},{3,7},{4,0},{5,1},{6,2},{7,3},{8,12},{9,13},{10,... | collective-permute-start | bytes 442376 | tf_op jit(solution)/shard_map/ppermute | solution.py:218
  25.6 3.5 %copy-start.6 = (bf16[2,9,32,128]{3,2,1,0:T(8,128)(2,1)}, bf16[2,9,32,128]{3,2,1,0:T(8,128)(2,1)S(1)}, u32[]{:S(2)}) copy-start(bf16[2,9,32,128]{3,2,1,0:T(8,128)(2,1)S(1)} %collective-permute-done.4.refs_3_) | copy-start | bytes 442372
  25.6 10.7 %collective-permute-start.5 = (bf16[2,9,32,128]{3,2,1,0:T(8,128)(2,1)S(1)}, bf16[2,9,32,128]{3,2,1,0:T(8,128)(2,1)S(1)}, u32[]{:S(2)}, u32[]{:S(2)}) collective-permute-start(bf16[2,9,32,128]{3,2,1,0:T(8,128)(2,1)S(1)} %collective-permute-done.4.refs_3_), channel_id=1, source_target_pairs={{0,8},{1,9},{2,10},{3,11},{4,12},{5,13},{6,14},{7,15},{8,0},{9,1},... | collective-permute-start | bytes 442376 | tf_op jit(solution)/shard_map/ppermute | solution.py:218
  27.8 5.6 %collective-permute-start.7 = (bf16[1,32,256]{2,1,0:T(8,128)(2,1)S(1)}, bf16[1,32,256]{2,1,0:T(8,128)(2,1)S(1)}, u32[]{:S(2)}, u32[]{:S(2)}) collective-permute-start(bf16[1,32,256]{2,1,0:T(8,128)(2,1)S(1)} %get-tuple-element.84), channel_id=1, source_target_pairs={{1,0},{2,1},{3,2},{4,3},{5,4},{6,5},{7,6},{8,7},{9,8},{10,9},{11,1... | collective-permute-start | bytes 49160 | tf_op jit(solution)/shard_map/ppermute | solution.py:324
  29.1 4.9 %collective-permute-start.6 = (bf16[1,32,256]{2,1,0:T(8,128)(2,1)S(1)}, bf16[1,32,256]{2,1,0:T(8,128)(2,1)S(1)}, u32[]{:S(2)}, u32[]{:S(2)}) collective-permute-start(bf16[1,32,256]{2,1,0:T(8,128)(2,1)S(1)} %get-tuple-element.85), channel_id=1, source_target_pairs={{0,1},{1,2},{2,3},{3,4},{4,5},{5,6},{6,7},{7,8},{8,9},{9,10},{10,1... | collective-permute-start | bytes 49160 | tf_op jit(solution)/shard_map/ppermute | solution.py:323
  32.2 10.4 %collective-permute-start.10 = (bf16[2,9,32,128]{3,2,1,0:T(8,128)(2,1)S(1)}, bf16[2,9,32,128]{3,2,1,0:T(8,128)(2,1)}, u32[]{:S(2)}, u32[]{:S(2)}) collective-permute-start(bf16[2,9,32,128]{3,2,1,0:T(8,128)(2,1)S(1)} %pad_maximum_fusion.refs_0_), channel_id=1, source_target_pairs={{0,1},{1,0},{2,3},{3,2},{4,5},{5,4},{6,7},{7,6},{8,9},{9,8},{10,11... | collective-permute-start | bytes 442376 | tf_op jit(solution)/shard_map/ppermute | solution.py:221
  33.4 9.8 %collective-permute-start.11 = (bf16[2,9,32,128]{3,2,1,0:T(8,128)(2,1)}, bf16[2,9,32,128]{3,2,1,0:T(8,128)(2,1)}, u32[]{:S(2)}, u32[]{:S(2)}) collective-permute-start(bf16[2,9,32,128]{3,2,1,0:T(8,128)(2,1)} %collective-permute-done.1.refs_1_), channel_id=1, source_target_pairs={{0,1},{1,0},{2,3},{3,2},{4,5},{5,4},{6,7},{7,6},{8,9},{9,8},{10,11... | collective-permute-start | bytes 442376 | tf_op jit(solution)/shard_map/ppermute | solution.py:221
  33.4 10.4 %collective-permute-start.9 = (bf16[2,9,32,128]{3,2,1,0:T(8,128)(2,1)}, bf16[2,9,32,128]{3,2,1,0:T(8,128)(2,1)}, u32[]{:S(2)}, u32[]{:S(2)}) collective-permute-start(bf16[2,9,32,128]{3,2,1,0:T(8,128)(2,1)} %collective-permute-done.2.refs_2_), channel_id=1, source_target_pairs={{0,8},{1,9},{2,10},{3,11},{4,12},{5,13},{6,14},{7,15},{8,0},{9,1},... | collective-permute-start | bytes 442376 | tf_op jit(solution)/shard_map/ppermute | solution.py:218
  34.0 9.8 %collective-permute-start.8 = (bf16[2,9,32,128]{3,2,1,0:T(8,128)(2,1)}, bf16[2,9,32,128]{3,2,1,0:T(8,128)(2,1)}, u32[]{:S(2)}, u32[]{:S(2)}) collective-permute-start(bf16[2,9,32,128]{3,2,1,0:T(8,128)(2,1)} %collective-permute-done.3.refs_4_), channel_id=1, source_target_pairs={{0,2},{1,3},{2,0},{3,1},{4,6},{5,7},{6,4},{7,5},{8,10},{9,11},{10,... | collective-permute-start | bytes 442376 | tf_op jit(solution)/shard_map/ppermute | solution.py:218
  37.0 7.3 %collective-permute-start.12 = (bf16[2,9,32,128]{3,2,1,0:T(8,128)(2,1)}, bf16[2,9,32,128]{3,2,1,0:T(8,128)(2,1)}, u32[]{:S(2)}, u32[]{:S(2)}) collective-permute-start(bf16[2,9,32,128]{3,2,1,0:T(8,128)(2,1)} %collective-permute-done.2.refs_2_), channel_id=1, source_target_pairs={{0,1},{1,0},{2,3},{3,2},{4,5},{5,4},{6,7},{7,6},{8,9},{9,8},{10,11... | collective-permute-start | bytes 442376 | tf_op jit(solution)/shard_map/ppermute | solution.py:221
  42.4 2.0 %copy-start.11 = (s32[128]{0:T(128)S(1)}, s32[128]{0:T(128)}, u32[]{:S(2)}) copy-start(s32[128]{0:T(128)} %param.14) | copy-start | bytes 1540
  42.4 3.3 %copy-start.1 = (bf16[128,96,96]{2,1,0:T(8,128)(2,1)S(1)}, bf16[128,96,96]{2,1,0:T(8,128)(2,1)}, u32[]{:S(2)}) copy-start(bf16[128,96,96]{2,1,0:T(8,128)(2,1)} %copy.10.coupling_ref) | copy-start | bytes 7077892
  42.6 1.9 %collective-permute-start.14 = (bf16[2,9,32,128]{3,2,1,0:T(8,128)(2,1)}, bf16[2,9,32,128]{3,2,1,0:T(8,128)(2,1)S(1)}, u32[]{:S(2)}, u32[]{:S(2)}) collective-permute-start(bf16[2,9,32,128]{3,2,1,0:T(8,128)(2,1)} %collective-permute-done.3.refs_4_), channel_id=1, source_target_pairs={{0,1},{1,0},{2,3},{3,2},{4,5},{5,4},{6,7},{7,6},{8,9},{9,8},{10,11... | collective-permute-start | bytes 442376 | tf_op jit(solution)/shard_map/ppermute | solution.py:221
  43.3 1.6 %collective-permute-start.13 = (bf16[2,9,32,128]{3,2,1,0:T(8,128)(2,1)S(1)}, bf16[2,9,32,128]{3,2,1,0:T(8,128)(2,1)S(1)}, u32[]{:S(2)}, u32[]{:S(2)}) collective-permute-start(bf16[2,9,32,128]{3,2,1,0:T(8,128)(2,1)S(1)} %copy-done.7), channel_id=1, source_target_pairs={{0,1},{1,0},{2,3},{3,2},{4,5},{5,4},{6,7},{7,6},{8,9},{9,8},{10,11... | collective-permute-start | bytes 442376 | tf_op jit(solution)/shard_map/ppermute | solution.py:221
  43.8 1.6 %collective-permute-start.16 = (bf16[2,9,32,128]{3,2,1,0:T(8,128)(2,1)}, bf16[2,9,32,128]{3,2,1,0:T(8,128)(2,1)S(1)}, u32[]{:S(2)}, u32[]{:S(2)}) collective-permute-start(bf16[2,9,32,128]{3,2,1,0:T(8,128)(2,1)} %collective-permute-done.9.refs_6_), channel_id=1, source_target_pairs={{0,1},{1,0},{2,3},{3,2},{4,5},{5,4},{6,7},{7,6},{8,9},{9,8},{10,11... | collective-permute-start | bytes 442376 | tf_op jit(solution)/shard_map/ppermute | solution.py:221
  43.8 1.8 %collective-permute-start.15 = (bf16[2,9,32,128]{3,2,1,0:T(8,128)(2,1)}, bf16[2,9,32,128]{3,2,1,0:T(8,128)(2,1)S(1)}, u32[]{:S(2)}, u32[]{:S(2)}) collective-permute-start(bf16[2,9,32,128]{3,2,1,0:T(8,128)(2,1)} %collective-permute-done.8.refs_5_), channel_id=1, source_target_pairs={{0,1},{1,0},{2,3},{3,2},{4,5},{5,4},{6,7},{7,6},{8,9},{9,8},{10,11... | collective-permute-start | bytes 442376 | tf_op jit(solution)/shard_map/ppermute | solution.py:221
  44.3 1.4 collective-permute-start.17
  51.9 25.5 %copy-start.2 = (bf16[8,96,256]{2,1,0:T(8,128)(2,1)S(1)}, bf16[8,96,256]{2,1,0:T(8,128)(2,1)}, u32[]{:S(2)}) copy-start(bf16[8,96,256]{2,1,0:T(8,128)(2,1)} %basis_ref.3) | copy-start | bytes 1179652
  51.9 25.5 %copy-start.3 = (bf16[8,96,96]{2,1,0:T(8,128)(2,1)S(1)}, bf16[8,96,96]{2,1,0:T(8,128)(2,1)}, u32[]{:S(2)}) copy-start(bf16[8,96,96]{2,1,0:T(8,128)(2,1)} %transfer_ref.3) | copy-start | bytes 442372
  51.9 25.5 %copy-start.10 = (s32[12]{0:T(128)S(1)}, s32[12]{0:T(128)}, u32[]{:S(2)}) copy-start(s32[12]{0:T(128)} %ranks_ref.5) | copy-start | bytes 148
  51.9 2.1 %collective-permute-start.19 = (bf16[4,2,9,32,128]{4,3,2,1,0:T(8,128)(2,1)S(1)}, bf16[4,2,9,32,128]{4,3,2,1,0:T(8,128)(2,1)S(1)}, u32[]{:S(2)}, u32[]{:S(2)}) collective-permute-start(bf16[4,2,9,32,128]{4,3,2,1,0:T(8,128)(2,1)S(1)} %get-tuple-element.51), channel_id=1, source_target_pairs={{0,1},{1,0},{2,3},{3,2},{4,5},{5,4},{6,7},{7,6},{8,9},{9,8},{10,11... | collective-permute-start | bytes 1769480 | tf_op jit(solution)/shard_map/ppermute | solution.py:221
  52.2 9.9 %collective-permute-start.18 = (bf16[4,2,9,32,128]{4,3,2,1,0:T(8,128)(2,1)S(1)}, bf16[4,2,9,32,128]{4,3,2,1,0:T(8,128)(2,1)S(1)}, u32[]{:S(2)}, u32[]{:S(2)}) collective-permute-start(bf16[4,2,9,32,128]{4,3,2,1,0:T(8,128)(2,1)S(1)} %get-tuple-element.49), channel_id=1, source_target_pairs={{0,1},{1,0},{2,3},{3,2},{4,5},{5,4},{6,7},{7,6},{8,9},{9,8},{10,11... | collective-permute-start | bytes 1769480 | tf_op jit(solution)/shard_map/ppermute | solution.py:221
  54.1 6.7 %collective-permute-start.22 = (bf16[2,9,32,128]{3,2,1,0:T(8,128)(2,1)S(1)}, bf16[2,9,32,128]{3,2,1,0:T(8,128)(2,1)S(1)}, u32[]{:S(2)}, u32[]{:S(2)}) collective-permute-start(bf16[2,9,32,128]{3,2,1,0:T(8,128)(2,1)S(1)} %get-tuple-element.56), channel_id=1, source_target_pairs={{0,8},{1,9},{2,10},{3,11},{4,12},{5,13},{6,14},{7,15},{8,0},{9,1},... | collective-permute-start | bytes 442376 | tf_op jit(solution)/shard_map/ppermute | solution.py:218
  55.1 8.3 %collective-permute-start.20 = (bf16[2,9,32,128]{3,2,1,0:T(8,128)(2,1)S(1)}, bf16[2,9,32,128]{3,2,1,0:T(8,128)(2,1)S(1)}, u32[]{:S(2)}, u32[]{:S(2)}) collective-permute-start(bf16[2,9,32,128]{3,2,1,0:T(8,128)(2,1)S(1)} %get-tuple-element.52), channel_id=1, source_target_pairs={{0,8},{1,9},{2,10},{3,11},{4,12},{5,13},{6,14},{7,15},{8,0},{9,1},... | collective-permute-start | bytes 442376 | tf_op jit(solution)/shard_map/ppermute | solution.py:218
  56.2 7.1 %collective-permute-start.21 = (bf16[2,9,32,128]{3,2,1,0:T(8,128)(2,1)S(1)}, bf16[2,9,32,128]{3,2,1,0:T(8,128)(2,1)S(1)}, u32[]{:S(2)}, u32[]{:S(2)}) collective-permute-start(bf16[2,9,32,128]{3,2,1,0:T(8,128)(2,1)S(1)} %get-tuple-element.53), channel_id=1, source_target_pairs={{0,2},{1,3},{2,0},{3,1},{4,6},{5,7},{6,4},{7,5},{8,10},{9,11},{10,... | collective-permute-start | bytes 442376 | tf_op jit(solution)/shard_map/ppermute | solution.py:218
  60.9 5.8 %collective-permute-start.23 = (bf16[2,9,32,128]{3,2,1,0:T(8,128)(2,1)S(1)}, bf16[2,9,32,128]{3,2,1,0:T(8,128)(2,1)S(1)}, u32[]{:S(2)}, u32[]{:S(2)}) collective-permute-start(bf16[2,9,32,128]{3,2,1,0:T(8,128)(2,1)S(1)} %add_convert_fusion.1), channel_id=1, source_target_pairs={{0,4},{1,5},{2,6},{3,7},{4,0},{5,1},{6,2},{7,3},{8,12},{9,13},{10,... | collective-permute-start | bytes 442376 | tf_op jit(solution)/shard_map/ppermute | solution.py:218
  63.5 5.8 %collective-permute-start.25 = (bf16[2,9,32,128]{3,2,1,0:T(8,128)(2,1)S(1)}, bf16[2,9,32,128]{3,2,1,0:T(8,128)(2,1)S(1)}, u32[]{:S(2)}, u32[]{:S(2)}) collective-permute-start(bf16[2,9,32,128]{3,2,1,0:T(8,128)(2,1)S(1)} %get-tuple-element.57), channel_id=1, source_target_pairs={{0,4},{1,5},{2,6},{3,7},{4,0},{5,1},{6,2},{7,3},{8,12},{9,13},{10,... | collective-permute-start | bytes 442376 | tf_op jit(solution)/shard_map/ppermute | solution.py:218
  64.7 5.1 %collective-permute-start.26 = (bf16[2,9,32,128]{3,2,1,0:T(8,128)(2,1)S(1)}, bf16[2,9,32,128]{3,2,1,0:T(8,128)(2,1)S(1)}, u32[]{:S(2)}, u32[]{:S(2)}) collective-permute-start(bf16[2,9,32,128]{3,2,1,0:T(8,128)(2,1)S(1)} %get-tuple-element.58), channel_id=1, source_target_pairs={{0,8},{1,9},{2,10},{3,11},{4,12},{5,13},{6,14},{7,15},{8,0},{9,1},... | collective-permute-start | bytes 442376 | tf_op jit(solution)/shard_map/ppermute | solution.py:218
  66.8 5.2 %collective-permute-start.24 = (bf16[2,9,32,128]{3,2,1,0:T(8,128)(2,1)S(1)}, bf16[2,9,32,128]{3,2,1,0:T(8,128)(2,1)S(1)}, u32[]{:S(2)}, u32[]{:S(2)}) collective-permute-start(bf16[2,9,32,128]{3,2,1,0:T(8,128)(2,1)S(1)} %shard_map.101), channel_id=1, source_target_pairs={{0,2},{1,3},{2,0},{3,1},{4,6},{5,7},{6,4},{7,5},{8,10},{9,11},{10,... | collective-permute-start | bytes 442376 | tf_op jit(solution)/shard_map/ppermute | solution.py:218
  72.1 5.3 %collective-permute-start.27 = (bf16[9,32,128]{2,1,0:T(8,128)(2,1)S(1)}, bf16[9,32,128]{2,1,0:T(8,128)(2,1)S(1)}, u32[]{:S(2)}, u32[]{:S(2)}) collective-permute-start(bf16[9,32,128]{2,1,0:T(8,128)(2,1)S(1)} %get-tuple-element.60), channel_id=1, source_target_pairs={{0,16},{1,17},{2,18},{3,19},{4,20},{5,21},{6,22},{7,23},{8,24},{9,... | collective-permute-start | bytes 221192 | tf_op jit(solution)/shard_map/ppermute | solution.py:215
  79.9 5.4 %collective-permute-start.28 = (bf16[9,32,128]{2,1,0:T(8,128)(2,1)S(1)}, bf16[9,32,128]{2,1,0:T(8,128)(2,1)S(1)}, u32[]{:S(2)}, u32[]{:S(2)}) collective-permute-start(bf16[9,32,128]{2,1,0:T(8,128)(2,1)S(1)} %get-tuple-element.62), channel_id=1, source_target_pairs={{0,16},{1,17},{2,18},{3,19},{4,20},{5,21},{6,22},{7,23},{8,24},{9,... | collective-permute-start | bytes 221192 | tf_op jit(solution)/shard_map/ppermute | solution.py:215
  85.3 5.2 %collective-permute-start.31 = (bf16[2,9,32,128]{3,2,1,0:T(8,128)(2,1)S(1)}, bf16[2,9,32,128]{3,2,1,0:T(8,128)(2,1)S(1)}, u32[]{:S(2)}, u32[]{:S(2)}) collective-permute-start(bf16[2,9,32,128]{3,2,1,0:T(8,128)(2,1)S(1)} %pad_maximum_fusion.1.refs_0_), channel_id=1, source_target_pairs={{0,8},{1,9},{2,10},{3,11},{4,12},{5,13},{6,14},{7,15},{8,0},{9,1},... | collective-permute-start | bytes 442376 | tf_op jit(solution)/shard_map/ppermute | solution.py:218
  87.4 5.1 %collective-permute-start.30 = (bf16[2,9,32,128]{3,2,1,0:T(8,128)(2,1)S(1)}, bf16[2,9,32,128]{3,2,1,0:T(8,128)(2,1)S(1)}, u32[]{:S(2)}, u32[]{:S(2)}) collective-permute-start(bf16[2,9,32,128]{3,2,1,0:T(8,128)(2,1)S(1)} %pad_maximum_fusion.1.refs_0_), channel_id=1, source_target_pairs={{0,4},{1,5},{2,6},{3,7},{4,0},{5,1},{6,2},{7,3},{8,12},{9,13},{10,... | collective-permute-start | bytes 442376 | tf_op jit(solution)/shard_map/ppermute | solution.py:218
  88.3 5.1 %collective-permute-start.29 = (bf16[2,9,32,128]{3,2,1,0:T(8,128)(2,1)S(1)}, bf16[2,9,32,128]{3,2,1,0:T(8,128)(2,1)S(1)}, u32[]{:S(2)}, u32[]{:S(2)}) collective-permute-start(bf16[2,9,32,128]{3,2,1,0:T(8,128)(2,1)S(1)} %pad_maximum_fusion.1.refs_0_), channel_id=1, source_target_pairs={{0,2},{1,3},{2,0},{3,1},{4,6},{5,7},{6,4},{7,5},{8,10},{9,11},{10,... | collective-permute-start | bytes 442376 | tf_op jit(solution)/shard_map/ppermute | solution.py:218
  93.4 5.1 %collective-permute-start.32 = (bf16[2,9,32,128]{3,2,1,0:T(8,128)(2,1)S(1)}, bf16[2,9,32,128]{3,2,1,0:T(8,128)(2,1)S(1)}, u32[]{:S(2)}, u32[]{:S(2)}) collective-permute-start(bf16[2,9,32,128]{3,2,1,0:T(8,128)(2,1)S(1)} %collective-permute-done.29.refs_1_), channel_id=1, source_target_pairs={{0,4},{1,5},{2,6},{3,7},{4,0},{5,1},{6,2},{7,3},{8,12},{9,13},{10,... | collective-permute-start | bytes 442376 | tf_op jit(solution)/shard_map/ppermute | solution.py:218
  98.5 10.3 %collective-permute-start.33 = (bf16[2,9,32,128]{3,2,1,0:T(8,128)(2,1)S(1)}, bf16[2,9,32,128]{3,2,1,0:T(8,128)(2,1)S(1)}, u32[]{:S(2)}, u32[]{:S(2)}) collective-permute-start(bf16[2,9,32,128]{3,2,1,0:T(8,128)(2,1)S(1)} %collective-permute-done.32.refs_3_), channel_id=1, source_target_pairs={{0,8},{1,9},{2,10},{3,11},{4,12},{5,13},{6,14},{7,15},{8,0},{9,1},... | collective-permute-start | bytes 442376 | tf_op jit(solution)/shard_map/ppermute | solution.py:218
  100.8 5.2 %collective-permute-start.35 = (bf16[1,32,256]{2,1,0:T(8,128)(2,1)S(1)}, bf16[1,32,256]{2,1,0:T(8,128)(2,1)S(1)}, u32[]{:S(2)}, u32[]{:S(2)}) collective-permute-start(bf16[1,32,256]{2,1,0:T(8,128)(2,1)S(1)} %get-tuple-element.82), channel_id=1, source_target_pairs={{1,0},{2,1},{3,2},{4,3},{5,4},{6,5},{7,6},{8,7},{9,8},{10,9},{11,1... | collective-permute-start | bytes 49160 | tf_op jit(solution)/shard_map/ppermute | solution.py:324
  102.1 4.6 %collective-permute-start.34 = (bf16[1,32,256]{2,1,0:T(8,128)(2,1)S(1)}, bf16[1,32,256]{2,1,0:T(8,128)(2,1)S(1)}, u32[]{:S(2)}, u32[]{:S(2)}) collective-permute-start(bf16[1,32,256]{2,1,0:T(8,128)(2,1)S(1)} %get-tuple-element.83), channel_id=1, source_target_pairs={{0,1},{1,2},{2,3},{3,4},{4,5},{5,6},{6,7},{7,8},{8,9},{9,10},{10,1... | collective-permute-start | bytes 49160 | tf_op jit(solution)/shard_map/ppermute | solution.py:323
  105.2 5.4 %collective-permute-start.38 = (bf16[2,9,32,128]{3,2,1,0:T(8,128)(2,1)S(1)}, bf16[2,9,32,128]{3,2,1,0:T(8,128)(2,1)S(1)}, u32[]{:S(2)}, u32[]{:S(2)}) collective-permute-start(bf16[2,9,32,128]{3,2,1,0:T(8,128)(2,1)S(1)} %pad_maximum_fusion.1.refs_0_), channel_id=1, source_target_pairs={{0,1},{1,0},{2,3},{3,2},{4,5},{5,4},{6,7},{7,6},{8,9},{9,8},{10,11... | collective-permute-start | bytes 442376 | tf_op jit(solution)/shard_map/ppermute | solution.py:221
  105.9 5.2 %collective-permute-start.39 = (bf16[2,9,32,128]{3,2,1,0:T(8,128)(2,1)S(1)}, bf16[2,9,32,128]{3,2,1,0:T(8,128)(2,1)S(1)}, u32[]{:S(2)}, u32[]{:S(2)}) collective-permute-start(bf16[2,9,32,128]{3,2,1,0:T(8,128)(2,1)S(1)} %collective-permute-done.29.refs_1_), channel_id=1, source_target_pairs={{0,1},{1,0},{2,3},{3,2},{4,5},{5,4},{6,7},{7,6},{8,9},{9,8},{10,11... | collective-permute-start | bytes 442376 | tf_op jit(solution)/shard_map/ppermute | solution.py:221
  106.0 6.2 %collective-permute-start.37 = (bf16[2,9,32,128]{3,2,1,0:T(8,128)(2,1)S(1)}, bf16[2,9,32,128]{3,2,1,0:T(8,128)(2,1)S(1)}, u32[]{:S(2)}, u32[]{:S(2)}) collective-permute-start(bf16[2,9,32,128]{3,2,1,0:T(8,128)(2,1)S(1)} %collective-permute-done.30.refs_2_), channel_id=1, source_target_pairs={{0,8},{1,9},{2,10},{3,11},{4,12},{5,13},{6,14},{7,15},{8,0},{9,1},... | collective-permute-start | bytes 442376 | tf_op jit(solution)/shard_map/ppermute | solution.py:218
  106.7 5.9 %collective-permute-start.36 = (bf16[2,9,32,128]{3,2,1,0:T(8,128)(2,1)S(1)}, bf16[2,9,32,128]{3,2,1,0:T(8,128)(2,1)S(1)}, u32[]{:S(2)}, u32[]{:S(2)}) collective-permute-start(bf16[2,9,32,128]{3,2,1,0:T(8,128)(2,1)S(1)} %collective-permute-done.31.refs_4_), channel_id=1, source_target_pairs={{0,2},{1,3},{2,0},{3,1},{4,6},{5,7},{6,4},{7,5},{8,10},{9,11},{10,... | collective-permute-start | bytes 442376 | tf_op jit(solution)/shard_map/ppermute | solution.py:218
  108.9 3.8 %collective-permute-start.40 = (bf16[2,9,32,128]{3,2,1,0:T(8,128)(2,1)S(1)}, bf16[2,9,32,128]{3,2,1,0:T(8,128)(2,1)S(1)}, u32[]{:S(2)}, u32[]{:S(2)}) collective-permute-start(bf16[2,9,32,128]{3,2,1,0:T(8,128)(2,1)S(1)} %collective-permute-done.30.refs_2_), channel_id=1, source_target_pairs={{0,1},{1,0},{2,3},{3,2},{4,5},{5,4},{6,7},{7,6},{8,9},{9,8},{10,11... | collective-permute-start | bytes 442376 | tf_op jit(solution)/shard_map/ppermute | solution.py:221
  110.6 2.6 %collective-permute-start.42 = (bf16[2,9,32,128]{3,2,1,0:T(8,128)(2,1)S(1)}, bf16[2,9,32,128]{3,2,1,0:T(8,128)(2,1)S(1)}, u32[]{:S(2)}, u32[]{:S(2)}) collective-permute-start(bf16[2,9,32,128]{3,2,1,0:T(8,128)(2,1)S(1)} %collective-permute-done.31.refs_4_), channel_id=1, source_target_pairs={{0,1},{1,0},{2,3},{3,2},{4,5},{5,4},{6,7},{7,6},{8,9},{9,8},{10,11... | collective-permute-start | bytes 442376 | tf_op jit(solution)/shard_map/ppermute | solution.py:221
  111.1 2.0 %collective-permute-start.41 = (bf16[2,9,32,128]{3,2,1,0:T(8,128)(2,1)S(1)}, bf16[2,9,32,128]{3,2,1,0:T(8,128)(2,1)S(1)}, u32[]{:S(2)}, u32[]{:S(2)}) collective-permute-start(bf16[2,9,32,128]{3,2,1,0:T(8,128)(2,1)S(1)} %collective-permute-done.32.refs_3_), channel_id=1, source_target_pairs={{0,1},{1,0},{2,3},{3,2},{4,5},{5,4},{6,7},{7,6},{8,9},{9,8},{10,11... | collective-permute-start | bytes 442376 | tf_op jit(solution)/shard_map/ppermute | solution.py:221
  112.2 1.4 collective-permute-start.44
  112.6 1.4 collective-permute-start.43
  112.7 1.5 %collective-permute-start.45 = (bf16[2,9,32,128]{3,2,1,0:T(8,128)(2,1)S(1)}, bf16[2,9,32,128]{3,2,1,0:T(8,128)(2,1)S(1)}, u32[]{:S(2)}, u32[]{:S(2)}) collective-permute-start(bf16[2,9,32,128]{3,2,1,0:T(8,128)(2,1)S(1)} %collective-permute-done.33.refs_7_), channel_id=1, source_target_pairs={{0,1},{1,0},{2,3},{3,2},{4,5},{5,4},{6,7},{7,6},{8,9},{9,8},{10,11... | collective-permute-start | bytes 442376 | tf_op jit(solution)/shard_map/ppermute | solution.py:221
  119.6 2.1 %collective-permute-start.47 = (bf16[4,2,9,32,128]{4,3,2,1,0:T(8,128)(2,1)S(1)}, bf16[4,2,9,32,128]{4,3,2,1,0:T(8,128)(2,1)S(1)}, u32[]{:S(2)}, u32[]{:S(2)}) collective-permute-start(bf16[4,2,9,32,128]{4,3,2,1,0:T(8,128)(2,1)S(1)} %get-tuple-element.72), channel_id=1, source_target_pairs={{0,1},{1,0},{2,3},{3,2},{4,5},{5,4},{6,7},{7,6},{8,9},{9,8},{10,11... | collective-permute-start | bytes 1769480 | tf_op jit(solution)/shard_map/ppermute | solution.py:221
  120.0 10.6 %collective-permute-start.46 = (bf16[4,2,9,32,128]{4,3,2,1,0:T(8,128)(2,1)S(1)}, bf16[4,2,9,32,128]{4,3,2,1,0:T(8,128)(2,1)S(1)}, u32[]{:S(2)}, u32[]{:S(2)}) collective-permute-start(bf16[4,2,9,32,128]{4,3,2,1,0:T(8,128)(2,1)S(1)} %get-tuple-element.70), channel_id=1, source_target_pairs={{0,1},{1,0},{2,3},{3,2},{4,5},{5,4},{6,7},{7,6},{8,9},{9,8},{10,11... | collective-permute-start | bytes 1769480 | tf_op jit(solution)/shard_map/ppermute | solution.py:221
  121.8 7.3 %collective-permute-start.50 = (bf16[2,9,32,128]{3,2,1,0:T(8,128)(2,1)S(1)}, bf16[2,9,32,128]{3,2,1,0:T(8,128)(2,1)S(1)}, u32[]{:S(2)}, u32[]{:S(2)}) collective-permute-start(bf16[2,9,32,128]{3,2,1,0:T(8,128)(2,1)S(1)} %get-tuple-element.77), channel_id=1, source_target_pairs={{0,8},{1,9},{2,10},{3,11},{4,12},{5,13},{6,14},{7,15},{8,0},{9,1},... | collective-permute-start | bytes 442376 | tf_op jit(solution)/shard_map/ppermute | solution.py:218
  124.5 7.5 %collective-permute-start.48 = (bf16[2,9,32,128]{3,2,1,0:T(8,128)(2,1)S(1)}, bf16[2,9,32,128]{3,2,1,0:T(8,128)(2,1)S(1)}, u32[]{:S(2)}, u32[]{:S(2)}) collective-permute-start(bf16[2,9,32,128]{3,2,1,0:T(8,128)(2,1)S(1)} %get-tuple-element.73), channel_id=1, source_target_pairs={{0,8},{1,9},{2,10},{3,11},{4,12},{5,13},{6,14},{7,15},{8,0},{9,1},... | collective-permute-start | bytes 442376 | tf_op jit(solution)/shard_map/ppermute | solution.py:218
  124.5 7.4 %collective-permute-start.49 = (bf16[2,9,32,128]{3,2,1,0:T(8,128)(2,1)S(1)}, bf16[2,9,32,128]{3,2,1,0:T(8,128)(2,1)S(1)}, u32[]{:S(2)}, u32[]{:S(2)}) collective-permute-start(bf16[2,9,32,128]{3,2,1,0:T(8,128)(2,1)S(1)} %get-tuple-element.74), channel_id=1, source_target_pairs={{0,2},{1,3},{2,0},{3,1},{4,6},{5,7},{6,4},{7,5},{8,10},{9,11},{10,... | collective-permute-start | bytes 442376 | tf_op jit(solution)/shard_map/ppermute | solution.py:218
  129.1 5.3 %collective-permute-start.51 = (bf16[2,9,32,128]{3,2,1,0:T(8,128)(2,1)S(1)}, bf16[2,9,32,128]{3,2,1,0:T(8,128)(2,1)S(1)}, u32[]{:S(2)}, u32[]{:S(2)}) collective-permute-start(bf16[2,9,32,128]{3,2,1,0:T(8,128)(2,1)S(1)} %add_convert_fusion), channel_id=1, source_target_pairs={{0,4},{1,5},{2,6},{3,7},{4,0},{5,1},{6,2},{7,3},{8,12},{9,13},{10,... | collective-permute-start | bytes 442376 | tf_op jit(solution)/shard_map/ppermute | solution.py:218
  132.1 5.6 %collective-permute-start.53 = (bf16[2,9,32,128]{3,2,1,0:T(8,128)(2,1)S(1)}, bf16[2,9,32,128]{3,2,1,0:T(8,128)(2,1)S(1)}, u32[]{:S(2)}, u32[]{:S(2)}) collective-permute-start(bf16[2,9,32,128]{3,2,1,0:T(8,128)(2,1)S(1)} %get-tuple-element.78), channel_id=1, source_target_pairs={{0,4},{1,5},{2,6},{3,7},{4,0},{5,1},{6,2},{7,3},{8,12},{9,13},{10,... | collective-permute-start | bytes 442376 | tf_op jit(solution)/shard_map/ppermute | solution.py:218
  133.2 5.1 %collective-permute-start.54 = (bf16[2,9,32,128]{3,2,1,0:T(8,128)(2,1)S(1)}, bf16[2,9,32,128]{3,2,1,0:T(8,128)(2,1)S(1)}, u32[]{:S(2)}, u32[]{:S(2)}) collective-permute-start(bf16[2,9,32,128]{3,2,1,0:T(8,128)(2,1)S(1)} %get-tuple-element.79), channel_id=1, source_target_pairs={{0,8},{1,9},{2,10},{3,11},{4,12},{5,13},{6,14},{7,15},{8,0},{9,1},... | collective-permute-start | bytes 442376 | tf_op jit(solution)/shard_map/ppermute | solution.py:218
  134.5 5.2 %collective-permute-start.52 = (bf16[2,9,32,128]{3,2,1,0:T(8,128)(2,1)S(1)}, bf16[2,9,32,128]{3,2,1,0:T(8,128)(2,1)S(1)}, u32[]{:S(2)}, u32[]{:S(2)}) collective-permute-start(bf16[2,9,32,128]{3,2,1,0:T(8,128)(2,1)S(1)} %shard_map.109), channel_id=1, source_target_pairs={{0,2},{1,3},{2,0},{3,1},{4,6},{5,7},{6,4},{7,5},{8,10},{9,11},{10,... | collective-permute-start | bytes 442376 | tf_op jit(solution)/shard_map/ppermute | solution.py:218
  139.8 5.3 %collective-permute-start.55 = (bf16[9,32,128]{2,1,0:T(8,128)(2,1)S(1)}, bf16[9,32,128]{2,1,0:T(8,128)(2,1)S(1)}, u32[]{:S(2)}, u32[]{:S(2)}) collective-permute-start(bf16[9,32,128]{2,1,0:T(8,128)(2,1)S(1)} %get-tuple-element.81), channel_id=1, source_target_pairs={{0,16},{1,17},{2,18},{3,19},{4,20},{5,21},{6,22},{7,23},{8,24},{9,... | collective-permute-start | bytes 221192 | tf_op jit(solution)/shard_map/ppermute | solution.py:215
  (5 other events, 6.5 us)

commit v6 on v5

--- a/solution.py
+++ b/solution.py
@@ -134,9 +134,11 @@
         out_ref[i] = total
 
 
-def edge_kernel(before_ref, after_ref, first_ref, last_ref, out_ref):
-    out_ref[0] = dot(before_ref[0], first_ref[0, 0])
-    out_ref[1] = dot(after_ref[0], last_ref[0, 0])
+def edge_kernel(core_ref, inner_ref, outer_ref, first_ref, last_ref, out_ref):
+    inner, outer = inner_ref[0], outer_ref[0]
+    even = core_ref[0] == 0
+    out_ref[0] = dot(jnp.where(even, outer, inner), first_ref[0, 0])
+    out_ref[1] = dot(jnp.where(even, inner, outer), last_ref[0, 0])
 
 
 def first_add_kernel(keep_ref, swap_ref, *out_refs):
@@ -144,11 +146,11 @@
         out_ref[...] = (keep_ref[n].astype(F32) + swap_ref[n].astype(F32)).astype(BF)
 
 
-def second_add_kernel(keep_ref, swap_ref, y_ref, z_ref, own_out, y_out, z_out):
+def second_add_kernel(keep_ref, swap_ref, yz_ref, zx_ref, own_out, y_out, z_out):
     own_out[...] = keep_ref[0].astype(F32) + swap_ref[0].astype(F32)
-    for n, part_ref, out_ref in ((2, y_ref, y_out), (3, z_ref, z_out)):
-        total = keep_ref[n].astype(F32) + swap_ref[n].astype(F32) + part_ref[...].astype(F32)
-        out_ref[...] = total.astype(BF)
+    y_out[...] = (keep_ref[2].astype(F32) + swap_ref[2].astype(F32)).astype(BF)
+    total = keep_ref[3].astype(F32) + swap_ref[3].astype(F32)
+    z_out[...] = (total + yz_ref[...].astype(F32) + zx_ref[...].astype(F32)).astype(BF)
 
 
 def third_add_kernel(keep_ref, swap_ref, x_ref, x_out):
@@ -280,6 +282,7 @@
         out_shape=shape((2, rhs, width), F32),
         grid=(1,),
         in_specs=[
+            SMEM,
             VMEM,
             VMEM,
             pl.BlockSpec((1, 1, width, width), lambda i: (0, 0, 0, 0)),
@@ -313,29 +316,47 @@
             compiler_params=params(16),
         )
 
-    ends = devices - 1
+    core = me % cores
+    barrier = lax.optimization_barrier
+
+    def halo(field_in):
+        head, tail = field_in[:1], field_in[leaves - 1 :]
+        inner = swap_cores(jnp.where(core == 0, tail, head))
+        pairs = [(d, d + 1) for d in range(1, devices - 1, 2)]
+        outer = lax.ppermute(
+            jnp.where(core == 0, head, tail), "clu", pairs + [(b, a) for a, b in pairs]
+        )
+        return inner, outer
 
     def apply_matrix(field_in, coeffs, with_coeffs):
-        got = {0: jnp.stack([coeffs] + [swap_far(coeffs, s) for s in range(1, far)])}
-        got[x], got[y], got[z] = lax.optimization_barrier((swap(got[0], x), swap(got[0], y), swap(got[0], z)))
-        got[x | y], got[y | z], got[z | x] = swap(got[x], y), swap(got[y], z), swap(got[z], x)
-        got[x | y | z] = swap(got[x | y], z)
-        before = lax.ppermute(field_in[leaves - 1 :], "clu", [(i, i + 1) for i in range(ends)])
-        after = lax.ppermute(field_in[:1], "clu", [(i + 1, i) for i in range(ends)])
+        away = [swap_far(coeffs, s) for s in range(1, far)]
+        away, inner, outer = barrier((away, *halo(field_in)))
+        got = {0: jnp.stack([coeffs] + away)}
+        got[x], got[y], got[z] = barrier((swap(got[0], x), swap(got[0], y), swap(got[0], z)))
         near_sum = near(field_in, near_field)
-        edges = edge(before, after, near_field, near_field)
-        got[7], near_sum, edges = lax.optimization_barrier((got[7], near_sum, edges))
-        own = [got[chip] for chip in range(chips)]
-        other = [swap_cores(part) for part in own]
-        keep_first, keep, send_first, send = couple(source_rows, target_rows, coupling, *own, *other)
-        far_corner, xy, yz, zx = first_add(keep_first, swap_cores(send_first))
+        got[x | y], got[y | z], got[z | x], near_sum = barrier(
+            (swap(got[x], y), swap(got[y], z), swap(got[z], x), near_sum)
+        )
+        edges = edge(core.reshape(1), inner, outer, near_field, near_field)
+        other = {chip: swap_cores(got[chip]) for chip in (0, x, y, z)}
+        got[x | y | z], edges, other = barrier((swap(got[x | y], z), edges, other))
+        for chip in (x | y, y | z, z | x, x | y | z):
+            other[chip] = swap_cores(got[chip])
+        keep_first, keep, send_first, send = couple(
+            source_rows,
+            target_rows,
+            coupling,
+            *[got[chip] for chip in range(chips)],
+            *[other[chip] for chip in range(chips)],
+        )
+        corner, xy, yz, zx = first_add(keep_first, swap_cores(send_first))
         swapped = swap_cores(send)
-        yz, zx = swap(yz, z), swap(zx, x)
-        xy = (xy.astype(F32) + swap(far_corner, z).astype(F32)).astype(BF)
-        xy = swap(xy, y)
+        corner, yz, zx = barrier((swap(corner, z), swap(yz, y), swap(zx, x)))
+        xy = swap((xy.astype(F32) + corner.astype(F32)).astype(BF), y)
         mine, to_y, to_z = second_add(keep, swapped, yz, zx)
+        to_y, to_z = swap(to_y, y), swap(to_z, z)
         (to_x,) = third_add(keep, swapped, xy)
-        total, *away = last_add(mine, swap(to_x, x), swap(to_y, y), swap(to_z, z))
+        total, *away = last_add(mine, swap(to_x, x), to_y, to_z)
         terms = [swap_far(part, s + 1) for s, part in enumerate(away)]
         return finish(with_coeffs)(ranks, near_sum, edges, basis, transfer, total, *terms)
 

time: 148 us -> 143 us (0.966)
  starting transfers between devices: 58.1 us -> 50.9 us
  local copies, waits for them, and re-layouts: 8.03 us -> 11.1 us
  waiting for transfers between devices: 57.9 us -> 55.5 us
    ppermute x4 -> x2, starting transfers between devices: 8.62 us -> 1.3 us  [halo(): lax.ppermute(jnp.where(core == 0, head, tail), 'clu', pairs + [(b, a) for...]
    ppermute x4, waiting for transfers between devices: 13.5 us -> 8.52 us  [swap_far(): lax.ppermute(part, 'clu', [(d, (d + shift * cube) % devices) for d in ran...]
    unnamed x27 -> x29, local copies, waits for them, and re-layouts: 6.56 us -> 11.1 us
    ppermute x20 -> x22, starting transfers between devices: 6.08 us -> 9.68 us  [swap_cores(): return lax.ppermute(part, 'clu', [(d, d ^ 1) for d in range(devices)])]
    ppermute x4, starting transfers between devices: 10.7 us -> 7.58 us  [swap_far(): lax.ppermute(part, 'clu', [(d, (d + shift * cube) % devices) for d in ran...]
    select_n x0 -> x2, other arithmetic: none -> 1.48 us  [halo(): jnp.where(core == 0, head, tail)]
    ppermute x20 -> x22, waiting for transfers between devices: 5.31 us -> 6.67 us  [swap_cores(): return lax.ppermute(part, 'clu', [(d, d ^ 1) for d in range(devices)])]
  transfers between devices with their start and end apart: 56 -> 56, of which waited for: 35 -> 34; matrix products, arithmetic and copies ran while one was open for 4% -> 4% of each run, Pallas kernels for 1% -> 2%
where the time goes in v6:
time: 143 us
  waiting for transfers between devices  55.5 us (39%)
  starting transfers between devices  50.9 us (36%)
  Pallas kernels  21.8 us (15%)
  local copies, waits for them, and re-layouts  11.1 us (8%)
  other arithmetic  2.53 us (2%)
    ppermute x28, waiting for transfers between devices, swap(): lax.ppermute(part, 'clu', [(d, d ^ chip * cores) for d in range(devices)])  40.3 us
    ppermute x28, starting transfers between devices, swap(): lax.ppermute(part, 'clu', [(d, d ^ chip * cores) for d in range(devices)])  32.3 us
    pallas_call x2, Pallas kernels, apply_matrix(): couple(source_rows, target_rows, coupling, *[got[chip] for chip in range(...  11.7 us
    unnamed x29, local copies, waits for them, and re-layouts  11.1 us
    ppermute x22, starting transfers between devices, swap_cores(): return lax.ppermute(part, 'clu', [(d, d ^ 1) for d in range(devices)])  9.68 us
    ppermute x4, waiting for transfers between devices, swap_far(): lax.ppermute(part, 'clu', [(d, (d + shift * cube) % devices) for d in ran...  8.52 us
    ppermute x4, starting transfers between devices, swap_far(): lax.ppermute(part, 'clu', [(d, (d + shift * cube) % devices) for d in ran...  7.58 us
    ppermute x22, waiting for transfers between devices, swap_cores(): return lax.ppermute(part, 'clu', [(d, d ^ 1) for d in range(devices)])  6.67 us
  transfers between devices with their start and end apart: 56, of which 34 were waited for; matrix products, arithmetic and copies ran while one was open for 4% of the time, Pallas kernels for 2%

profile of v6, /device:TPU:0, one launch (start us, length us, event | category | flops | bytes accessed | tf_op | source)
XLA Modules:
  0.0 142.7 jit_solution(11392676801227763036)
XLA Ops:
  0.6 2.9 %shard_map.95 = bf16[9,32,128]{2,1,0:T(8,128)(2,1)} custom-call(s32[12]{0:T(128)} %ranks_ref.5, bf16[8,32,256]{2,1,0:T(8,128)(2,1)} %v_ref.1, bf16[8,96,256]{2,1,0:T(8,128)(2,1)} %basis_ref.3, bf16[8,96,96]{2,1,0:T(8,128)(2,1)} %transfer_ref.3), custom_call_target="tpu_custom_call" | custom-call | tf_op jit(solution)/shard_map/pallas_call | solution.py:240
  3.5 4.1 %collective-permute-start = (bf16[9,32,128]{2,1,0:T(8,128)(2,1)}, bf16[9,32,128]{2,1,0:T(8,128)(2,1)S(1)}, u32[]{:S(2)}, u32[]{:S(2)}) collective-permute-start(bf16[9,32,128]{2,1,0:T(8,128)(2,1)} %shard_map.95), channel_id=1, source_target_pairs={{0,16},{1,17},{2,18},{3,19},{4,20},{5,21},{6,22},{7,23},{8,24},{9,... | collective-permute-start | bytes 221192 | tf_op jit(solution)/shard_map/ppermute | solution.py:217
  7.6 0.7 broadcast_select_fusion.2
  8.4 0.7 collective-permute-start.2
  9.0 2.9 %collective-permute-start.1 = (bf16[1,32,256]{2,1,0:T(8,128)(2,1)S(1)}, bf16[1,32,256]{2,1,0:T(8,128)(2,1)S(1)}, u32[]{:S(2)}, u32[]{:S(2)}) collective-permute-start(bf16[1,32,256]{2,1,0:T(8,128)(2,1)S(1)} %get-tuple-element.137), channel_id=1, source_target_pairs={{0,1},{1,0},{2,3},{3,2},{4,5},{5,4},{6,7},{7,6},{8,9},{9,8},{10,11... | collective-permute-start | bytes 49160 | tf_op jit(solution)/shard_map/ppermute | solution.py:223
  12.0 0.6 copy-done.7
  12.8 0.6 copy-done.9
  13.4 0.9 pad_maximum_fusion.refs_0_
  14.3 4.7 %collective-permute-start.5 = (bf16[2,9,32,128]{3,2,1,0:T(8,128)(2,1)S(1)}, bf16[2,9,32,128]{3,2,1,0:T(8,128)(2,1)}, u32[]{:S(2)}, u32[]{:S(2)}) collective-permute-start(bf16[2,9,32,128]{3,2,1,0:T(8,128)(2,1)S(1)} %pad_maximum_fusion.refs_0_), channel_id=1, source_target_pairs={{0,8},{1,9},{2,10},{3,11},{4,12},{5,13},{6,14},{7,15},{8,0},{9,1},... | collective-permute-start | bytes 442376 | tf_op jit(solution)/shard_map/ppermute | solution.py:220
  19.0 0.6 collective-permute-start.4
  19.6 0.6 collective-permute-start.3
  20.2 2.0 %collective-permute-done.5.refs_4_ = bf16[2,9,32,128]{3,2,1,0:T(8,128)(2,1)} collective-permute-done((bf16[2,9,32,128]{3,2,1,0:T(8,128)(2,1)S(1)}, bf16[2,9,32,128]{3,2,1,0:T(8,128)(2,1)}, u32[]{:S(2)}, u32[]{:S(2)}) %collective-permute-start.5) | collective-permute-done | bytes 147488 | tf_op jit(solution)/shard_map/ppermute | solution.py:220
  22.2 2.0 %collective-permute-done.4.refs_2_ = bf16[2,9,32,128]{3,2,1,0:T(8,128)(2,1)} collective-permute-done((bf16[2,9,32,128]{3,2,1,0:T(8,128)(2,1)S(1)}, bf16[2,9,32,128]{3,2,1,0:T(8,128)(2,1)}, u32[]{:S(2)}, u32[]{:S(2)}) %collective-permute-start.4) | collective-permute-done | bytes 147488 | tf_op jit(solution)/shard_map/ppermute | solution.py:220
  24.2 0.9 collective-permute-done.3.refs_1_
  25.1 1.2 collective-permute-start.6
  26.3 1.2 collective-permute-start.8
  27.6 1.9 %copy-done = bf16[8,3,256,256]{3,2,1,0:T(8,128)(2,1)S(1)} copy-done((bf16[8,3,256,256]{3,2,1,0:T(8,128)(2,1)S(1)}, bf16[8,3,256,256]{3,2,1,0:T(8,128)(2,1)}, u32[]{:S(2)}) %copy-start) | copy-done | bytes 3145752
  29.5 0.9 copy-done.5
  32.0 1.7 %collective-permute-start.9 = (bf16[2,9,32,128]{3,2,1,0:T(8,128)(2,1)}, bf16[2,9,32,128]{3,2,1,0:T(8,128)(2,1)}, u32[]{:S(2)}, u32[]{:S(2)}) collective-permute-start(bf16[2,9,32,128]{3,2,1,0:T(8,128)(2,1)} %collective-permute-done.6.refs_3_), channel_id=1, source_target_pairs={{0,8},{1,9},{2,10},{3,11},{4,12},{5,13},{6,14},{7,15},{8,0},{9,1},... | collective-permute-start | bytes 442376 | tf_op jit(solution)/shard_map/ppermute | solution.py:220
  33.7 4.8 %copy.10.coupling_ref = bf16[128,96,96]{2,1,0:T(8,128)(2,1)} copy(bf16[128,96,96]{0,2,1:T(8,128)(2,1)} %param.12) | data formatting | bytes 4718592 | tf_op args[4]
  38.5 0.7 copy-done.8
  39.2 0.7 copy-done.10
  41.2 0.7 collective-permute-done.15.refs_13_
  42.5 6.3 %shard_map.98 = (bf16[4,2,9,32,128]{4,3,2,1,0:T(8,128)(2,1)S(1)}, bf16[4,2,9,32,128]{4,3,2,1,0:T(8,128)(2,1)S(1)}, bf16[4,2,9,32,128]{4,3,2,1,0:T(8,128)(2,1)S(1)}, bf16[4,2,9,32,128]{4,3,2,1,0:T(8,128)(2,1)S(1)}) custom-call(s32[128]{0:T(128)S(1)} %get-tuple-element.138.source_ref, s32[128]{0:T(128)S(1)} %get-tuple-element.139.target_ref, ...), custom_call_target="tpu_custom_call" | custom-call | flops 75497472 | bytes 10485760 | tf_op jit(solution)/shard_map/pallas_call | solution.py:345
  49.4 1.5 %collective-permute-done.19.swap_ref = bf16[4,2,9,32,128]{4,3,2,1,0:T(8,128)(2,1)S(1)} collective-permute-done((bf16[4,2,9,32,128]{4,3,2,1,0:T(8,128)(2,1)S(1)}, bf16[4,2,9,32,128]{4,3,2,1,0:T(8,128)(2,1)S(1)}, u32[]{:S(2)}, u32[]{:S(2)}) %collective-permute-start.19) | collective-permute-done | bytes 589856 | tf_op jit(solution)/shard_map/ppermute | solution.py:223
  51.4 1.7 %collective-permute-start.21 = (bf16[2,9,32,128]{3,2,1,0:T(8,128)(2,1)S(1)}, bf16[2,9,32,128]{3,2,1,0:T(8,128)(2,1)S(1)}, u32[]{:S(2)}, u32[]{:S(2)}) collective-permute-start(bf16[2,9,32,128]{3,2,1,0:T(8,128)(2,1)S(1)} %get-tuple-element.89), channel_id=1, source_target_pairs={{0,4},{1,5},{2,6},{3,7},{4,0},{5,1},{6,2},{7,3},{8,12},{9,13},{10,... | collective-permute-start | bytes 442376 | tf_op jit(solution)/shard_map/ppermute | solution.py:220
  53.2 1.0 collective-permute-start.22
  54.2 3.0 %collective-permute-done.20 = bf16[2,9,32,128]{3,2,1,0:T(8,128)(2,1)S(1)} collective-permute-done((bf16[2,9,32,128]{3,2,1,0:T(8,128)(2,1)S(1)}, bf16[2,9,32,128]{3,2,1,0:T(8,128)(2,1)S(1)}, u32[]{:S(2)}, u32[]{:S(2)}) %collective-permute-start.20) | collective-permute-done | bytes 147488 | tf_op jit(solution)/shard_map/ppermute | solution.py:220
  57.2 1.4 collective-permute-done.22.zx_ref
  59.3 1.8 %collective-permute-start.25 = (bf16[2,9,32,128]{3,2,1,0:T(8,128)(2,1)S(1)}, bf16[2,9,32,128]{3,2,1,0:T(8,128)(2,1)S(1)}, u32[]{:S(2)}, u32[]{:S(2)}) collective-permute-start(bf16[2,9,32,128]{3,2,1,0:T(8,128)(2,1)S(1)} %get-tuple-element.96), channel_id=1, source_target_pairs={{0,4},{1,5},{2,6},{3,7},{4,0},{5,1},{6,2},{7,3},{8,12},{9,13},{10,... | collective-permute-start | bytes 442376 | tf_op jit(solution)/shard_map/ppermute | solution.py:220
  61.0 1.6 %collective-permute-start.26 = (bf16[2,9,32,128]{3,2,1,0:T(8,128)(2,1)S(1)}, bf16[2,9,32,128]{3,2,1,0:T(8,128)(2,1)S(1)}, u32[]{:S(2)}, u32[]{:S(2)}) collective-permute-start(bf16[2,9,32,128]{3,2,1,0:T(8,128)(2,1)S(1)} %get-tuple-element.97), channel_id=1, source_target_pairs={{0,8},{1,9},{2,10},{3,11},{4,12},{5,13},{6,14},{7,15},{8,0},{9,1},... | collective-permute-start | bytes 442376 | tf_op jit(solution)/shard_map/ppermute | solution.py:220
  62.6 2.4 %collective-permute-done.23.x_ref = bf16[2,9,32,128]{3,2,1,0:T(8,128)(2,1)S(1)} collective-permute-done((bf16[2,9,32,128]{3,2,1,0:T(8,128)(2,1)S(1)}, bf16[2,9,32,128]{3,2,1,0:T(8,128)(2,1)S(1)}, u32[]{:S(2)}, u32[]{:S(2)}) %collective-permute-start.23) | collective-permute-done | bytes 147488 | tf_op jit(solution)/shard_map/ppermute | solution.py:220
  65.0 1.1 collective-permute-start.24
  66.6 3.7 %collective-permute-done.24.x_ref = bf16[2,9,32,128]{3,2,1,0:T(8,128)(2,1)S(1)} collective-permute-done((bf16[2,9,32,128]{3,2,1,0:T(8,128)(2,1)S(1)}, bf16[2,9,32,128]{3,2,1,0:T(8,128)(2,1)S(1)}, u32[]{:S(2)}, u32[]{:S(2)}) %collective-permute-start.24) | collective-permute-done | bytes 147488 | tf_op jit(solution)/shard_map/ppermute | solution.py:220
  70.7 4.9 %collective-permute-done.27.rest_0_ = bf16[9,32,128]{2,1,0:T(8,128)(2,1)S(1)} collective-permute-done((bf16[9,32,128]{2,1,0:T(8,128)(2,1)S(1)}, bf16[9,32,128]{2,1,0:T(8,128)(2,1)S(1)}, u32[]{:S(2)}, u32[]{:S(2)}) %collective-permute-start.27) | collective-permute-done | bytes 73760 | tf_op jit(solution)/shard_map/ppermute | solution.py:217
  75.6 2.5 %shard_map.103 = (bf16[8,32,256]{2,1,0:T(8,128)(2,1)}, bf16[9,32,128]{2,1,0:T(8,128)(2,1)S(1)}) custom-call(s32[12]{0:T(128)S(1)} %copy-done.11, f32[8,32,256]{2,1,0:T(8,128)S(1)} %shard_map.96.near_ref, f32[2,32,256]{2,1,0:T(8,128)S(1)} %shard_map.97.edge_ref, bf16[8,96,256]{2,1,0:T(8,128)(2,1)S(1)} %copy-done.3, bf16[8,96,96]{2,1,0:T(8,128)(2,1)S(1)} %copy-done.4, ...), custom_call_target="tpu_custom_call" | custom-call | tf_op jit(solution)/shard_map/pallas_call | solution.py:361
  78.6 0.7 broadcast_select_fusion
  79.3 0.7 collective-permute-start.30
  80.0 2.4 %collective-permute-start.29 = (bf16[1,32,256]{2,1,0:T(8,128)(2,1)S(1)}, bf16[1,32,256]{2,1,0:T(8,128)(2,1)S(1)}, u32[]{:S(2)}, u32[]{:S(2)}) collective-permute-start(bf16[1,32,256]{2,1,0:T(8,128)(2,1)S(1)} %get-tuple-element.135), channel_id=1, source_target_pairs={{0,1},{1,0},{2,3},{3,2},{4,5},{5,4},{6,7},{7,6},{8,9},{9,8},{10,11... | collective-permute-start | bytes 49160 | tf_op jit(solution)/shard_map/ppermute | solution.py:223
  82.4 0.8 collective-permute-done.29.inner_ref
  83.4 4.8 %collective-permute-start.33 = (bf16[2,9,32,128]{3,2,1,0:T(8,128)(2,1)S(1)}, bf16[2,9,32,128]{3,2,1,0:T(8,128)(2,1)S(1)}, u32[]{:S(2)}, u32[]{:S(2)}) collective-permute-start(bf16[2,9,32,128]{3,2,1,0:T(8,128)(2,1)S(1)} %pad_maximum_fusion.1.refs_0_), channel_id=1, source_target_pairs={{0,8},{1,9},{2,10},{3,11},{4,12},{5,13},{6,14},{7,15},{8,0},{9,1},... | collective-permute-start | bytes 442376 | tf_op jit(solution)/shard_map/ppermute | solution.py:220
  88.7 2.6 %collective-permute-done.33.refs_4_ = bf16[2,9,32,128]{3,2,1,0:T(8,128)(2,1)S(1)} collective-permute-done((bf16[2,9,32,128]{3,2,1,0:T(8,128)(2,1)S(1)}, bf16[2,9,32,128]{3,2,1,0:T(8,128)(2,1)S(1)}, u32[]{:S(2)}, u32[]{:S(2)}) %collective-permute-start.33) | collective-permute-done | bytes 147488 | tf_op jit(solution)/shard_map/ppermute | solution.py:220
  91.3 2.0 %collective-permute-done.32.refs_2_ = bf16[2,9,32,128]{3,2,1,0:T(8,128)(2,1)S(1)} collective-permute-done((bf16[2,9,32,128]{3,2,1,0:T(8,128)(2,1)S(1)}, bf16[2,9,32,128]{3,2,1,0:T(8,128)(2,1)S(1)}, u32[]{:S(2)}, u32[]{:S(2)}) %collective-permute-start.32) | collective-permute-done | bytes 147488 | tf_op jit(solution)/shard_map/ppermute | solution.py:220
  93.7 1.6 %collective-permute-start.34 = (bf16[2,9,32,128]{3,2,1,0:T(8,128)(2,1)S(1)}, bf16[2,9,32,128]{3,2,1,0:T(8,128)(2,1)S(1)}, u32[]{:S(2)}, u32[]{:S(2)}) collective-permute-start(bf16[2,9,32,128]{3,2,1,0:T(8,128)(2,1)S(1)} %collective-permute-done.31.refs_1_), channel_id=1, source_target_pairs={{0,4},{1,5},{2,6},{3,7},{4,0},{5,1},{6,2},{7,3},{8,12},{9,13},{10,... | collective-permute-start | bytes 442376 | tf_op jit(solution)/shard_map/ppermute | solution.py:220
  95.5 0.9 copy-done.6
  96.4 0.6 shard_map.104.near_ref
  97.5 1.4 collective-permute-done.34.refs_3_
  98.9 1.6 %collective-permute-done.35.refs_6_ = bf16[2,9,32,128]{3,2,1,0:T(8,128)(2,1)S(1)} collective-permute-done((bf16[2,9,32,128]{3,2,1,0:T(8,128)(2,1)S(1)}, bf16[2,9,32,128]{3,2,1,0:T(8,128)(2,1)S(1)}, u32[]{:S(2)}, u32[]{:S(2)}) %collective-permute-start.35) | collective-permute-done | bytes 147488 | tf_op jit(solution)/shard_map/ppermute | solution.py:220
  100.6 1.9 %collective-permute-start.37 = (bf16[2,9,32,128]{3,2,1,0:T(8,128)(2,1)S(1)}, bf16[2,9,32,128]{3,2,1,0:T(8,128)(2,1)S(1)}, u32[]{:S(2)}, u32[]{:S(2)}) collective-permute-start(bf16[2,9,32,128]{3,2,1,0:T(8,128)(2,1)S(1)} %collective-permute-done.34.refs_3_), channel_id=1, source_target_pairs={{0,8},{1,9},{2,10},{3,11},{4,12},{5,13},{6,14},{7,15},{8,0},{9,1},... | collective-permute-start | bytes 442376 | tf_op jit(solution)/shard_map/ppermute | solution.py:220
  103.4 3.4 %collective-permute-done.37.refs_7_ = bf16[2,9,32,128]{3,2,1,0:T(8,128)(2,1)S(1)} collective-permute-done((bf16[2,9,32,128]{3,2,1,0:T(8,128)(2,1)S(1)}, bf16[2,9,32,128]{3,2,1,0:T(8,128)(2,1)S(1)}, u32[]{:S(2)}, u32[]{:S(2)}) %collective-permute-start.37) | collective-permute-done | bytes 147488 | tf_op jit(solution)/shard_map/ppermute | solution.py:220
  106.8 1.3 collective-permute-done.45.refs_15_
  108.2 5.4 %shard_map.106 = (bf16[4,2,9,32,128]{4,3,2,1,0:T(8,128)(2,1)S(1)}, bf16[4,2,9,32,128]{4,3,2,1,0:T(8,128)(2,1)S(1)}, bf16[4,2,9,32,128]{4,3,2,1,0:T(8,128)(2,1)S(1)}, bf16[4,2,9,32,128]{4,3,2,1,0:T(8,128)(2,1)S(1)}) custom-call(s32[128]{0:T(128)S(1)} %get-tuple-element.138.source_ref, s32[128]{0:T(128)S(1)} %get-tuple-element.139.target_ref, ...), custom_call_target="tpu_custom_call" | custom-call | flops 75497472 | bytes 10485760 | tf_op jit(solution)/shard_map/pallas_call | solution.py:345
  114.1 1.5 %collective-permute-done.47.swap_ref = bf16[4,2,9,32,128]{4,3,2,1,0:T(8,128)(2,1)S(1)} collective-permute-done((bf16[4,2,9,32,128]{4,3,2,1,0:T(8,128)(2,1)S(1)}, bf16[4,2,9,32,128]{4,3,2,1,0:T(8,128)(2,1)S(1)}, u32[]{:S(2)}, u32[]{:S(2)}) %collective-permute-start.47) | collective-permute-done | bytes 589856 | tf_op jit(solution)/shard_map/ppermute | solution.py:223
  115.7 1.0 collective-permute-start.48
  117.4 4.3 %collective-permute-done.48 = bf16[2,9,32,128]{3,2,1,0:T(8,128)(2,1)S(1)} collective-permute-done((bf16[2,9,32,128]{3,2,1,0:T(8,128)(2,1)S(1)}, bf16[2,9,32,128]{3,2,1,0:T(8,128)(2,1)S(1)}, u32[]{:S(2)}, u32[]{:S(2)}) %collective-permute-start.48) | collective-permute-done | bytes 147488 | tf_op jit(solution)/shard_map/ppermute | solution.py:220
  121.7 0.6 collective-permute-done.49.yz_ref
  122.5 1.7 %collective-permute-start.51 = (bf16[2,9,32,128]{3,2,1,0:T(8,128)(2,1)S(1)}, bf16[2,9,32,128]{3,2,1,0:T(8,128)(2,1)S(1)}, u32[]{:S(2)}, u32[]{:S(2)}) collective-permute-start(bf16[2,9,32,128]{3,2,1,0:T(8,128)(2,1)S(1)} %add_convert_fusion), channel_id=1, source_target_pairs={{0,4},{1,5},{2,6},{3,7},{4,0},{5,1},{6,2},{7,3},{8,12},{9,13},{10,... | collective-permute-start | bytes 442376 | tf_op jit(solution)/shard_map/ppermute | solution.py:220
  124.8 1.1 collective-permute-start.54
  125.9 2.9 %collective-permute-done.51.x_ref = bf16[2,9,32,128]{3,2,1,0:T(8,128)(2,1)S(1)} collective-permute-done((bf16[2,9,32,128]{3,2,1,0:T(8,128)(2,1)S(1)}, bf16[2,9,32,128]{3,2,1,0:T(8,128)(2,1)S(1)}, u32[]{:S(2)}, u32[]{:S(2)}) %collective-permute-start.51) | collective-permute-done | bytes 147488 | tf_op jit(solution)/shard_map/ppermute | solution.py:220
  129.2 1.2 collective-permute-done.53.y_ref
  130.4 3.7 %collective-permute-done.52.x_ref = bf16[2,9,32,128]{3,2,1,0:T(8,128)(2,1)S(1)} collective-permute-done((bf16[2,9,32,128]{3,2,1,0:T(8,128)(2,1)S(1)}, bf16[2,9,32,128]{3,2,1,0:T(8,128)(2,1)S(1)}, u32[]{:S(2)}, u32[]{:S(2)}) %collective-permute-start.52) | collective-permute-done | bytes 147488 | tf_op jit(solution)/shard_map/ppermute | solution.py:220
  134.1 2.6 %collective-permute-start.55 = (bf16[9,32,128]{2,1,0:T(8,128)(2,1)S(1)}, bf16[9,32,128]{2,1,0:T(8,128)(2,1)S(1)}, u32[]{:S(2)}, u32[]{:S(2)}) collective-permute-start(bf16[9,32,128]{2,1,0:T(8,128)(2,1)S(1)} %get-tuple-element.133), channel_id=1, source_target_pairs={{0,16},{1,17},{2,18},{3,19},{4,20},{5,21},{6,22},{7,23},{8,24},{9,... | collective-permute-start | bytes 221192 | tf_op jit(solution)/shard_map/ppermute | solution.py:217
  136.8 3.5 %collective-permute-done.55.rest_0_ = bf16[9,32,128]{2,1,0:T(8,128)(2,1)S(1)} collective-permute-done((bf16[9,32,128]{2,1,0:T(8,128)(2,1)S(1)}, bf16[9,32,128]{2,1,0:T(8,128)(2,1)S(1)}, u32[]{:S(2)}, u32[]{:S(2)}) %collective-permute-start.55) | collective-permute-done | bytes 73760 | tf_op jit(solution)/shard_map/ppermute | solution.py:217
  140.2 2.5 %shard_map.111 = bf16[8,32,256]{2,1,0:T(8,128)(2,1)} custom-call(s32[12]{0:T(128)S(1)} %copy-done.11, f32[8,32,256]{2,1,0:T(8,128)S(1)} %shard_map.104.near_ref, f32[2,32,256]{2,1,0:T(8,128)S(1)} %shard_map.105.edge_ref, bf16[8,96,256]{2,1,0:T(8,128)(2,1)S(1)} %copy-done.3, bf16[8,96,96]{2,1,0:T(8,128)(2,1)S(1)} %copy-done.4, ...), custom_call_target="tpu_custom_call" | custom-call | tf_op jit(solution)/shard_map/pallas_call | solution.py:361
  (101 shorter events, 12.2 us)
Async XLA Ops:
  3.5 9.9 %collective-permute-start = (bf16[9,32,128]{2,1,0:T(8,128)(2,1)}, bf16[9,32,128]{2,1,0:T(8,128)(2,1)S(1)}, u32[]{:S(2)}, u32[]{:S(2)}) collective-permute-start(bf16[9,32,128]{2,1,0:T(8,128)(2,1)} %shard_map.95), channel_id=1, source_target_pairs={{0,16},{1,17},{2,18},{3,19},{4,20},{5,21},{6,22},{7,23},{8,24},{9,... | collective-permute-start | bytes 221192 | tf_op jit(solution)/shard_map/ppermute | solution.py:217
  8.4 3.6 %collective-permute-start.2 = (bf16[1,32,256]{2,1,0:T(8,128)(2,1)S(1)}, bf16[1,32,256]{2,1,0:T(8,128)(2,1)S(1)}, u32[]{:S(2)}, u32[]{:S(2)}) collective-permute-start(bf16[1,32,256]{2,1,0:T(8,128)(2,1)S(1)} %get-tuple-element.136), channel_id=1, source_target_pairs={{1,2},{3,4},{5,6},{7,8},{9,10},{11,12},{13,14},{15,16},{17,18},{19... | collective-permute-start | bytes 49160 | tf_op jit(solution)/shard_map/ppermute | solution.py:326
  9.0 3.8 %collective-permute-start.1 = (bf16[1,32,256]{2,1,0:T(8,128)(2,1)S(1)}, bf16[1,32,256]{2,1,0:T(8,128)(2,1)S(1)}, u32[]{:S(2)}, u32[]{:S(2)}) collective-permute-start(bf16[1,32,256]{2,1,0:T(8,128)(2,1)S(1)} %get-tuple-element.137), channel_id=1, source_target_pairs={{0,1},{1,0},{2,3},{3,2},{4,5},{5,4},{6,7},{7,6},{8,9},{9,8},{10,11... | collective-permute-start | bytes 49160 | tf_op jit(solution)/shard_map/ppermute | solution.py:223
  14.3 7.9 %collective-permute-start.5 = (bf16[2,9,32,128]{3,2,1,0:T(8,128)(2,1)S(1)}, bf16[2,9,32,128]{3,2,1,0:T(8,128)(2,1)}, u32[]{:S(2)}, u32[]{:S(2)}) collective-permute-start(bf16[2,9,32,128]{3,2,1,0:T(8,128)(2,1)S(1)} %pad_maximum_fusion.refs_0_), channel_id=1, source_target_pairs={{0,8},{1,9},{2,10},{3,11},{4,12},{5,13},{6,14},{7,15},{8,0},{9,1},... | collective-permute-start | bytes 442376 | tf_op jit(solution)/shard_map/ppermute | solution.py:220
  19.0 5.2 %collective-permute-start.4 = (bf16[2,9,32,128]{3,2,1,0:T(8,128)(2,1)S(1)}, bf16[2,9,32,128]{3,2,1,0:T(8,128)(2,1)}, u32[]{:S(2)}, u32[]{:S(2)}) collective-permute-start(bf16[2,9,32,128]{3,2,1,0:T(8,128)(2,1)S(1)} %pad_maximum_fusion.refs_0_), channel_id=1, source_target_pairs={{0,4},{1,5},{2,6},{3,7},{4,0},{5,1},{6,2},{7,3},{8,12},{9,13},{10,... | collective-permute-start | bytes 442376 | tf_op jit(solution)/shard_map/ppermute | solution.py:220
  19.6 5.5 %collective-permute-start.3 = (bf16[2,9,32,128]{3,2,1,0:T(8,128)(2,1)S(1)}, bf16[2,9,32,128]{3,2,1,0:T(8,128)(2,1)}, u32[]{:S(2)}, u32[]{:S(2)}) collective-permute-start(bf16[2,9,32,128]{3,2,1,0:T(8,128)(2,1)S(1)} %pad_maximum_fusion.refs_0_), channel_id=1, source_target_pairs={{0,2},{1,3},{2,0},{3,1},{4,6},{5,7},{6,4},{7,5},{8,10},{9,11},{10,... | collective-permute-start | bytes 442376 | tf_op jit(solution)/shard_map/ppermute | solution.py:220
  25.1 6.4 %collective-permute-start.6 = (bf16[2,9,32,128]{3,2,1,0:T(8,128)(2,1)}, bf16[2,9,32,128]{3,2,1,0:T(8,128)(2,1)}, u32[]{:S(2)}, u32[]{:S(2)}) collective-permute-start(bf16[2,9,32,128]{3,2,1,0:T(8,128)(2,1)} %collective-permute-done.3.refs_1_), channel_id=1, source_target_pairs={{0,4},{1,5},{2,6},{3,7},{4,0},{5,1},{6,2},{7,3},{8,12},{9,13},{10,... | collective-permute-start | bytes 442376 | tf_op jit(solution)/shard_map/ppermute | solution.py:220
  26.2 5.5 %collective-permute-start.7 = (bf16[2,9,32,128]{3,2,1,0:T(8,128)(2,1)}, bf16[2,9,32,128]{3,2,1,0:T(8,128)(2,1)}, u32[]{:S(2)}, u32[]{:S(2)}) collective-permute-start(bf16[2,9,32,128]{3,2,1,0:T(8,128)(2,1)} %collective-permute-done.4.refs_2_), channel_id=1, source_target_pairs={{0,8},{1,9},{2,10},{3,11},{4,12},{5,13},{6,14},{7,15},{8,0},{9,1},... | collective-permute-start | bytes 442376 | tf_op jit(solution)/shard_map/ppermute | solution.py:220
  26.3 5.7 %collective-permute-start.8 = (bf16[2,9,32,128]{3,2,1,0:T(8,128)(2,1)}, bf16[2,9,32,128]{3,2,1,0:T(8,128)(2,1)}, u32[]{:S(2)}, u32[]{:S(2)}) collective-permute-start(bf16[2,9,32,128]{3,2,1,0:T(8,128)(2,1)} %collective-permute-done.5.refs_4_), channel_id=1, source_target_pairs={{0,2},{1,3},{2,0},{3,1},{4,6},{5,7},{6,4},{7,5},{8,10},{9,11},{10,... | collective-permute-start | bytes 442376 | tf_op jit(solution)/shard_map/ppermute | solution.py:220
  27.6 1.9 %copy-start = (bf16[8,3,256,256]{3,2,1,0:T(8,128)(2,1)S(1)}, bf16[8,3,256,256]{3,2,1,0:T(8,128)(2,1)}, u32[]{:S(2)}) copy-start(bf16[8,3,256,256]{3,2,1,0:T(8,128)(2,1)} %last_ref.3) | copy-start | bytes 9437188
  31.0 7.5 %copy-start.1 = (bf16[8,3,256,256]{3,2,1,0:T(8,128)(2,1)S(1)}, bf16[8,3,256,256]{3,2,1,0:T(8,128)(2,1)}, u32[]{:S(2)}) copy-start(bf16[8,3,256,256]{3,2,1,0:T(8,128)(2,1)} %last_ref.3) | copy-start | bytes 9437188
  31.0 9.1 %collective-permute-start.10 = (bf16[2,9,32,128]{3,2,1,0:T(8,128)(2,1)S(1)}, bf16[2,9,32,128]{3,2,1,0:T(8,128)(2,1)}, u32[]{:S(2)}, u32[]{:S(2)}) collective-permute-start(bf16[2,9,32,128]{3,2,1,0:T(8,128)(2,1)S(1)} %pad_maximum_fusion.refs_0_), channel_id=1, source_target_pairs={{0,1},{1,0},{2,3},{3,2},{4,5},{5,4},{6,7},{7,6},{8,9},{9,8},{10,11... | collective-permute-start | bytes 442376 | tf_op jit(solution)/shard_map/ppermute | solution.py:223
  31.0 9.2 %collective-permute-start.11 = (bf16[2,9,32,128]{3,2,1,0:T(8,128)(2,1)}, bf16[2,9,32,128]{3,2,1,0:T(8,128)(2,1)}, u32[]{:S(2)}, u32[]{:S(2)}) collective-permute-start(bf16[2,9,32,128]{3,2,1,0:T(8,128)(2,1)} %collective-permute-done.3.refs_1_), channel_id=1, source_target_pairs={{0,1},{1,0},{2,3},{3,2},{4,5},{5,4},{6,7},{7,6},{8,9},{9,8},{10,11... | collective-permute-start | bytes 442376 | tf_op jit(solution)/shard_map/ppermute | solution.py:223
  31.5 9.2 %collective-permute-start.12 = (bf16[2,9,32,128]{3,2,1,0:T(8,128)(2,1)}, bf16[2,9,32,128]{3,2,1,0:T(8,128)(2,1)}, u32[]{:S(2)}, u32[]{:S(2)}) collective-permute-start(bf16[2,9,32,128]{3,2,1,0:T(8,128)(2,1)} %collective-permute-done.4.refs_2_), channel_id=1, source_target_pairs={{0,1},{1,0},{2,3},{3,2},{4,5},{5,4},{6,7},{7,6},{8,9},{9,8},{10,11... | collective-permute-start | bytes 442376 | tf_op jit(solution)/shard_map/ppermute | solution.py:223
  31.7 9.0 %collective-permute-start.13 = (bf16[2,9,32,128]{3,2,1,0:T(8,128)(2,1)}, bf16[2,9,32,128]{3,2,1,0:T(8,128)(2,1)}, u32[]{:S(2)}, u32[]{:S(2)}) collective-permute-start(bf16[2,9,32,128]{3,2,1,0:T(8,128)(2,1)} %collective-permute-done.5.refs_4_), channel_id=1, source_target_pairs={{0,1},{1,0},{2,3},{3,2},{4,5},{5,4},{6,7},{7,6},{8,9},{9,8},{10,11... | collective-permute-start | bytes 442376 | tf_op jit(solution)/shard_map/ppermute | solution.py:223
  32.0 8.7 %collective-permute-start.9 = (bf16[2,9,32,128]{3,2,1,0:T(8,128)(2,1)}, bf16[2,9,32,128]{3,2,1,0:T(8,128)(2,1)}, u32[]{:S(2)}, u32[]{:S(2)}) collective-permute-start(bf16[2,9,32,128]{3,2,1,0:T(8,128)(2,1)} %collective-permute-done.6.refs_3_), channel_id=1, source_target_pairs={{0,8},{1,9},{2,10},{3,11},{4,12},{5,13},{6,14},{7,15},{8,0},{9,1},... | collective-permute-start | bytes 442376 | tf_op jit(solution)/shard_map/ppermute | solution.py:220
  39.9 1.3 copy-start.12
  39.9 1.3 copy-start.13
  39.9 2.5 %copy-start.2 = (bf16[128,96,96]{2,1,0:T(8,128)(2,1)S(1)}, bf16[128,96,96]{2,1,0:T(8,128)(2,1)}, u32[]{:S(2)}) copy-start(bf16[128,96,96]{2,1,0:T(8,128)(2,1)} %copy.10.coupling_ref) | copy-start | bytes 7077892
  40.1 2.2 %collective-permute-start.14 = (bf16[2,9,32,128]{3,2,1,0:T(8,128)(2,1)}, bf16[2,9,32,128]{3,2,1,0:T(8,128)(2,1)S(1)}, u32[]{:S(2)}, u32[]{:S(2)}) collective-permute-start(bf16[2,9,32,128]{3,2,1,0:T(8,128)(2,1)} %collective-permute-done.6.refs_3_), channel_id=1, source_target_pairs={{0,1},{1,0},{2,3},{3,2},{4,5},{5,4},{6,7},{7,6},{8,9},{9,8},{10,11... | collective-permute-start | bytes 442376 | tf_op jit(solution)/shard_map/ppermute | solution.py:223
  40.2 1.8 %collective-permute-start.15 = (bf16[2,9,32,128]{3,2,1,0:T(8,128)(2,1)}, bf16[2,9,32,128]{3,2,1,0:T(8,128)(2,1)S(1)}, u32[]{:S(2)}, u32[]{:S(2)}) collective-permute-start(bf16[2,9,32,128]{3,2,1,0:T(8,128)(2,1)} %collective-permute-done.8.refs_5_), channel_id=1, source_target_pairs={{0,1},{1,0},{2,3},{3,2},{4,5},{5,4},{6,7},{7,6},{8,9},{9,8},{10,11... | collective-permute-start | bytes 442376 | tf_op jit(solution)/shard_map/ppermute | solution.py:223
  40.7 1.6 %collective-permute-start.16 = (bf16[2,9,32,128]{3,2,1,0:T(8,128)(2,1)}, bf16[2,9,32,128]{3,2,1,0:T(8,128)(2,1)S(1)}, u32[]{:S(2)}, u32[]{:S(2)}) collective-permute-start(bf16[2,9,32,128]{3,2,1,0:T(8,128)(2,1)} %collective-permute-done.7.refs_6_), channel_id=1, source_target_pairs={{0,1},{1,0},{2,3},{3,2},{4,5},{5,4},{6,7},{7,6},{8,9},{9,8},{10,11... | collective-permute-start | bytes 442376 | tf_op jit(solution)/shard_map/ppermute | solution.py:223
  40.8 1.7 %collective-permute-start.17 = (bf16[2,9,32,128]{3,2,1,0:T(8,128)(2,1)}, bf16[2,9,32,128]{3,2,1,0:T(8,128)(2,1)S(1)}, u32[]{:S(2)}, u32[]{:S(2)}) collective-permute-start(bf16[2,9,32,128]{3,2,1,0:T(8,128)(2,1)} %collective-permute-done.9.refs_7_), channel_id=1, source_target_pairs={{0,1},{1,0},{2,3},{3,2},{4,5},{5,4},{6,7},{7,6},{8,9},{9,8},{10,11... | collective-permute-start | bytes 442376 | tf_op jit(solution)/shard_map/ppermute | solution.py:223
  48.8 26.9 %copy-start.3 = (bf16[8,96,256]{2,1,0:T(8,128)(2,1)S(1)}, bf16[8,96,256]{2,1,0:T(8,128)(2,1)}, u32[]{:S(2)}) copy-start(bf16[8,96,256]{2,1,0:T(8,128)(2,1)} %basis_ref.3) | copy-start | bytes 1179652
  48.8 26.8 %copy-start.4 = (bf16[8,96,96]{2,1,0:T(8,128)(2,1)S(1)}, bf16[8,96,96]{2,1,0:T(8,128)(2,1)}, u32[]{:S(2)}) copy-start(bf16[8,96,96]{2,1,0:T(8,128)(2,1)} %transfer_ref.3) | copy-start | bytes 442372
  48.8 26.8 %copy-start.11 = (s32[12]{0:T(128)S(1)}, s32[12]{0:T(128)}, u32[]{:S(2)}) copy-start(s32[12]{0:T(128)} %ranks_ref.5) | copy-start | bytes 148
  48.8 2.1 %collective-permute-start.19 = (bf16[4,2,9,32,128]{4,3,2,1,0:T(8,128)(2,1)S(1)}, bf16[4,2,9,32,128]{4,3,2,1,0:T(8,128)(2,1)S(1)}, u32[]{:S(2)}, u32[]{:S(2)}) collective-permute-start(bf16[4,2,9,32,128]{4,3,2,1,0:T(8,128)(2,1)S(1)} %get-tuple-element.87), channel_id=1, source_target_pairs={{0,1},{1,0},{2,3},{3,2},{4,5},{5,4},{6,7},{7,6},{8,9},{9,8},{10,11... | collective-permute-start | bytes 1769480 | tf_op jit(solution)/shard_map/ppermute | solution.py:223
  49.2 9.9 %collective-permute-start.18 = (bf16[4,2,9,32,128]{4,3,2,1,0:T(8,128)(2,1)S(1)}, bf16[4,2,9,32,128]{4,3,2,1,0:T(8,128)(2,1)S(1)}, u32[]{:S(2)}, u32[]{:S(2)}) collective-permute-start(bf16[4,2,9,32,128]{4,3,2,1,0:T(8,128)(2,1)S(1)} %get-tuple-element.85), channel_id=1, source_target_pairs={{0,1},{1,0},{2,3},{3,2},{4,5},{5,4},{6,7},{7,6},{8,9},{9,8},{10,11... | collective-permute-start | bytes 1769480 | tf_op jit(solution)/shard_map/ppermute | solution.py:223
  51.0 6.1 %collective-permute-start.20 = (bf16[2,9,32,128]{3,2,1,0:T(8,128)(2,1)S(1)}, bf16[2,9,32,128]{3,2,1,0:T(8,128)(2,1)S(1)}, u32[]{:S(2)}, u32[]{:S(2)}) collective-permute-start(bf16[2,9,32,128]{3,2,1,0:T(8,128)(2,1)S(1)} %get-tuple-element.88), channel_id=1, source_target_pairs={{0,8},{1,9},{2,10},{3,11},{4,12},{5,13},{6,14},{7,15},{8,0},{9,1},... | collective-permute-start | bytes 442376 | tf_op jit(solution)/shard_map/ppermute | solution.py:220
  51.4 5.8 %collective-permute-start.21 = (bf16[2,9,32,128]{3,2,1,0:T(8,128)(2,1)S(1)}, bf16[2,9,32,128]{3,2,1,0:T(8,128)(2,1)S(1)}, u32[]{:S(2)}, u32[]{:S(2)}) collective-permute-start(bf16[2,9,32,128]{3,2,1,0:T(8,128)(2,1)S(1)} %get-tuple-element.89), channel_id=1, source_target_pairs={{0,4},{1,5},{2,6},{3,7},{4,0},{5,1},{6,2},{7,3},{8,12},{9,13},{10,... | collective-permute-start | bytes 442376 | tf_op jit(solution)/shard_map/ppermute | solution.py:220
  53.2 5.5 %collective-permute-start.22 = (bf16[2,9,32,128]{3,2,1,0:T(8,128)(2,1)S(1)}, bf16[2,9,32,128]{3,2,1,0:T(8,128)(2,1)S(1)}, u32[]{:S(2)}, u32[]{:S(2)}) collective-permute-start(bf16[2,9,32,128]{3,2,1,0:T(8,128)(2,1)S(1)} %get-tuple-element.90), channel_id=1, source_target_pairs={{0,2},{1,3},{2,0},{3,1},{4,6},{5,7},{6,4},{7,5},{8,10},{9,11},{10,... | collective-permute-start | bytes 442376 | tf_op jit(solution)/shard_map/ppermute | solution.py:220
  58.7 6.3 %collective-permute-start.23 = (bf16[2,9,32,128]{3,2,1,0:T(8,128)(2,1)S(1)}, bf16[2,9,32,128]{3,2,1,0:T(8,128)(2,1)S(1)}, u32[]{:S(2)}, u32[]{:S(2)}) collective-permute-start(bf16[2,9,32,128]{3,2,1,0:T(8,128)(2,1)S(1)} %add_convert_fusion.1), channel_id=1, source_target_pairs={{0,4},{1,5},{2,6},{3,7},{4,0},{5,1},{6,2},{7,3},{8,12},{9,13},{10,... | collective-permute-start | bytes 442376 | tf_op jit(solution)/shard_map/ppermute | solution.py:220
  59.3 7.3 %collective-permute-start.25 = (bf16[2,9,32,128]{3,2,1,0:T(8,128)(2,1)S(1)}, bf16[2,9,32,128]{3,2,1,0:T(8,128)(2,1)S(1)}, u32[]{:S(2)}, u32[]{:S(2)}) collective-permute-start(bf16[2,9,32,128]{3,2,1,0:T(8,128)(2,1)S(1)} %get-tuple-element.96), channel_id=1, source_target_pairs={{0,4},{1,5},{2,6},{3,7},{4,0},{5,1},{6,2},{7,3},{8,12},{9,13},{10,... | collective-permute-start | bytes 442376 | tf_op jit(solution)/shard_map/ppermute | solution.py:220
  61.0 5.5 %collective-permute-start.26 = (bf16[2,9,32,128]{3,2,1,0:T(8,128)(2,1)S(1)}, bf16[2,9,32,128]{3,2,1,0:T(8,128)(2,1)S(1)}, u32[]{:S(2)}, u32[]{:S(2)}) collective-permute-start(bf16[2,9,32,128]{3,2,1,0:T(8,128)(2,1)S(1)} %get-tuple-element.97), channel_id=1, source_target_pairs={{0,8},{1,9},{2,10},{3,11},{4,12},{5,13},{6,14},{7,15},{8,0},{9,1},... | collective-permute-start | bytes 442376 | tf_op jit(solution)/shard_map/ppermute | solution.py:220
  65.0 5.2 %collective-permute-start.24 = (bf16[2,9,32,128]{3,2,1,0:T(8,128)(2,1)S(1)}, bf16[2,9,32,128]{3,2,1,0:T(8,128)(2,1)S(1)}, u32[]{:S(2)}, u32[]{:S(2)}) collective-permute-start(bf16[2,9,32,128]{3,2,1,0:T(8,128)(2,1)S(1)} %shard_map.101), channel_id=1, source_target_pairs={{0,2},{1,3},{2,0},{3,1},{4,6},{5,7},{6,4},{7,5},{8,10},{9,11},{10,... | collective-permute-start | bytes 442376 | tf_op jit(solution)/shard_map/ppermute | solution.py:220
  70.3 5.3 %collective-permute-start.27 = (bf16[9,32,128]{2,1,0:T(8,128)(2,1)S(1)}, bf16[9,32,128]{2,1,0:T(8,128)(2,1)S(1)}, u32[]{:S(2)}, u32[]{:S(2)}) collective-permute-start(bf16[9,32,128]{2,1,0:T(8,128)(2,1)S(1)} %get-tuple-element.99), channel_id=1, source_target_pairs={{0,16},{1,17},{2,18},{3,19},{4,20},{5,21},{6,22},{7,23},{8,24},{9,... | collective-permute-start | bytes 221192 | tf_op jit(solution)/shard_map/ppermute | solution.py:217
  78.1 5.3 %collective-permute-start.28 = (bf16[9,32,128]{2,1,0:T(8,128)(2,1)S(1)}, bf16[9,32,128]{2,1,0:T(8,128)(2,1)S(1)}, u32[]{:S(2)}, u32[]{:S(2)}) collective-permute-start(bf16[9,32,128]{2,1,0:T(8,128)(2,1)S(1)} %get-tuple-element.101), channel_id=1, source_target_pairs={{0,16},{1,17},{2,18},{3,19},{4,20},{5,21},{6,22},{7,23},{8,24},{9,... | collective-permute-start | bytes 221192 | tf_op jit(solution)/shard_map/ppermute | solution.py:217
  79.3 3.1 %collective-permute-start.30 = (bf16[1,32,256]{2,1,0:T(8,128)(2,1)S(1)}, bf16[1,32,256]{2,1,0:T(8,128)(2,1)S(1)}, u32[]{:S(2)}, u32[]{:S(2)}) collective-permute-start(bf16[1,32,256]{2,1,0:T(8,128)(2,1)S(1)} %get-tuple-element.134), channel_id=1, source_target_pairs={{1,2},{3,4},{5,6},{7,8},{9,10},{11,12},{13,14},{15,16},{17,18},{19... | collective-permute-start | bytes 49160 | tf_op jit(solution)/shard_map/ppermute | solution.py:326
  80.0 3.3 %collective-permute-start.29 = (bf16[1,32,256]{2,1,0:T(8,128)(2,1)S(1)}, bf16[1,32,256]{2,1,0:T(8,128)(2,1)S(1)}, u32[]{:S(2)}, u32[]{:S(2)}) collective-permute-start(bf16[1,32,256]{2,1,0:T(8,128)(2,1)S(1)} %get-tuple-element.135), channel_id=1, source_target_pairs={{0,1},{1,0},{2,3},{3,2},{4,5},{5,4},{6,7},{7,6},{8,9},{9,8},{10,11... | collective-permute-start | bytes 49160 | tf_op jit(solution)/shard_map/ppermute | solution.py:223
  83.4 7.9 %collective-permute-start.33 = (bf16[2,9,32,128]{3,2,1,0:T(8,128)(2,1)S(1)}, bf16[2,9,32,128]{3,2,1,0:T(8,128)(2,1)S(1)}, u32[]{:S(2)}, u32[]{:S(2)}) collective-permute-start(bf16[2,9,32,128]{3,2,1,0:T(8,128)(2,1)S(1)} %pad_maximum_fusion.1.refs_0_), channel_id=1, source_target_pairs={{0,8},{1,9},{2,10},{3,11},{4,12},{5,13},{6,14},{7,15},{8,0},{9,1},... | collective-permute-start | bytes 442376 | tf_op jit(solution)/shard_map/ppermute | solution.py:220
  88.2 5.1 %collective-permute-start.32 = (bf16[2,9,32,128]{3,2,1,0:T(8,128)(2,1)S(1)}, bf16[2,9,32,128]{3,2,1,0:T(8,128)(2,1)S(1)}, u32[]{:S(2)}, u32[]{:S(2)}) collective-permute-start(bf16[2,9,32,128]{3,2,1,0:T(8,128)(2,1)S(1)} %pad_maximum_fusion.1.refs_0_), channel_id=1, source_target_pairs={{0,4},{1,5},{2,6},{3,7},{4,0},{5,1},{6,2},{7,3},{8,12},{9,13},{10,... | collective-permute-start | bytes 442376 | tf_op jit(solution)/shard_map/ppermute | solution.py:220
  88.6 5.1 %collective-permute-start.31 = (bf16[2,9,32,128]{3,2,1,0:T(8,128)(2,1)S(1)}, bf16[2,9,32,128]{3,2,1,0:T(8,128)(2,1)S(1)}, u32[]{:S(2)}, u32[]{:S(2)}) collective-permute-start(bf16[2,9,32,128]{3,2,1,0:T(8,128)(2,1)S(1)} %pad_maximum_fusion.1.refs_0_), channel_id=1, source_target_pairs={{0,2},{1,3},{2,0},{3,1},{4,6},{5,7},{6,4},{7,5},{8,10},{9,11},{10,... | collective-permute-start | bytes 442376 | tf_op jit(solution)/shard_map/ppermute | solution.py:220
  93.7 5.1 %collective-permute-start.34 = (bf16[2,9,32,128]{3,2,1,0:T(8,128)(2,1)S(1)}, bf16[2,9,32,128]{3,2,1,0:T(8,128)(2,1)S(1)}, u32[]{:S(2)}, u32[]{:S(2)}) collective-permute-start(bf16[2,9,32,128]{3,2,1,0:T(8,128)(2,1)S(1)} %collective-permute-done.31.refs_1_), channel_id=1, source_target_pairs={{0,4},{1,5},{2,6},{3,7},{4,0},{5,1},{6,2},{7,3},{8,12},{9,13},{10,... | collective-permute-start | bytes 442376 | tf_op jit(solution)/shard_map/ppermute | solution.py:220
  95.4 5.1 %collective-permute-start.35 = (bf16[2,9,32,128]{3,2,1,0:T(8,128)(2,1)S(1)}, bf16[2,9,32,128]{3,2,1,0:T(8,128)(2,1)S(1)}, u32[]{:S(2)}, u32[]{:S(2)}) collective-permute-start(bf16[2,9,32,128]{3,2,1,0:T(8,128)(2,1)S(1)} %collective-permute-done.32.refs_2_), channel_id=1, source_target_pairs={{0,8},{1,9},{2,10},{3,11},{4,12},{5,13},{6,14},{7,15},{8,0},{9,1},... | collective-permute-start | bytes 442376 | tf_op jit(solution)/shard_map/ppermute | solution.py:220
  95.5 5.1 %collective-permute-start.36 = (bf16[2,9,32,128]{3,2,1,0:T(8,128)(2,1)S(1)}, bf16[2,9,32,128]{3,2,1,0:T(8,128)(2,1)S(1)}, u32[]{:S(2)}, u32[]{:S(2)}) collective-permute-start(bf16[2,9,32,128]{3,2,1,0:T(8,128)(2,1)S(1)} %collective-permute-done.33.refs_4_), channel_id=1, source_target_pairs={{0,2},{1,3},{2,0},{3,1},{4,6},{5,7},{6,4},{7,5},{8,10},{9,11},{10,... | collective-permute-start | bytes 442376 | tf_op jit(solution)/shard_map/ppermute | solution.py:220
  97.0 5.7 %collective-permute-start.38 = (bf16[2,9,32,128]{3,2,1,0:T(8,128)(2,1)S(1)}, bf16[2,9,32,128]{3,2,1,0:T(8,128)(2,1)S(1)}, u32[]{:S(2)}, u32[]{:S(2)}) collective-permute-start(bf16[2,9,32,128]{3,2,1,0:T(8,128)(2,1)S(1)} %pad_maximum_fusion.1.refs_0_), channel_id=1, source_target_pairs={{0,1},{1,0},{2,3},{3,2},{4,5},{5,4},{6,7},{7,6},{8,9},{9,8},{10,11... | collective-permute-start | bytes 442376 | tf_op jit(solution)/shard_map/ppermute | solution.py:223
  97.0 5.8 %collective-permute-start.39 = (bf16[2,9,32,128]{3,2,1,0:T(8,128)(2,1)S(1)}, bf16[2,9,32,128]{3,2,1,0:T(8,128)(2,1)S(1)}, u32[]{:S(2)}, u32[]{:S(2)}) collective-permute-start(bf16[2,9,32,128]{3,2,1,0:T(8,128)(2,1)S(1)} %collective-permute-done.31.refs_1_), channel_id=1, source_target_pairs={{0,1},{1,0},{2,3},{3,2},{4,5},{5,4},{6,7},{7,6},{8,9},{9,8},{10,11... | collective-permute-start | bytes 442376 | tf_op jit(solution)/shard_map/ppermute | solution.py:223
  98.9 4.4 %collective-permute-start.40 = (bf16[2,9,32,128]{3,2,1,0:T(8,128)(2,1)S(1)}, bf16[2,9,32,128]{3,2,1,0:T(8,128)(2,1)S(1)}, u32[]{:S(2)}, u32[]{:S(2)}) collective-permute-start(bf16[2,9,32,128]{3,2,1,0:T(8,128)(2,1)S(1)} %collective-permute-done.32.refs_2_), channel_id=1, source_target_pairs={{0,1},{1,0},{2,3},{3,2},{4,5},{5,4},{6,7},{7,6},{8,9},{9,8},{10,11... | collective-permute-start | bytes 442376 | tf_op jit(solution)/shard_map/ppermute | solution.py:223
  100.5 2.9 %collective-permute-start.41 = (bf16[2,9,32,128]{3,2,1,0:T(8,128)(2,1)S(1)}, bf16[2,9,32,128]{3,2,1,0:T(8,128)(2,1)S(1)}, u32[]{:S(2)}, u32[]{:S(2)}) collective-permute-start(bf16[2,9,32,128]{3,2,1,0:T(8,128)(2,1)S(1)} %collective-permute-done.33.refs_4_), channel_id=1, source_target_pairs={{0,1},{1,0},{2,3},{3,2},{4,5},{5,4},{6,7},{7,6},{8,9},{9,8},{10,11... | collective-permute-start | bytes 442376 | tf_op jit(solution)/shard_map/ppermute | solution.py:223
  100.6 6.2 %collective-permute-start.37 = (bf16[2,9,32,128]{3,2,1,0:T(8,128)(2,1)S(1)}, bf16[2,9,32,128]{3,2,1,0:T(8,128)(2,1)S(1)}, u32[]{:S(2)}, u32[]{:S(2)}) collective-permute-start(bf16[2,9,32,128]{3,2,1,0:T(8,128)(2,1)S(1)} %collective-permute-done.34.refs_3_), channel_id=1, source_target_pairs={{0,8},{1,9},{2,10},{3,11},{4,12},{5,13},{6,14},{7,15},{8,0},{9,1},... | collective-permute-start | bytes 442376 | tf_op jit(solution)/shard_map/ppermute | solution.py:220
  102.7 4.1 %collective-permute-start.42 = (bf16[2,9,32,128]{3,2,1,0:T(8,128)(2,1)S(1)}, bf16[2,9,32,128]{3,2,1,0:T(8,128)(2,1)S(1)}, u32[]{:S(2)}, u32[]{:S(2)}) collective-permute-start(bf16[2,9,32,128]{3,2,1,0:T(8,128)(2,1)S(1)} %collective-permute-done.34.refs_3_), channel_id=1, source_target_pairs={{0,1},{1,0},{2,3},{3,2},{4,5},{5,4},{6,7},{7,6},{8,9},{9,8},{10,11... | collective-permute-start | bytes 442376 | tf_op jit(solution)/shard_map/ppermute | solution.py:223
  102.8 4.0 %collective-permute-start.43 = (bf16[2,9,32,128]{3,2,1,0:T(8,128)(2,1)S(1)}, bf16[2,9,32,128]{3,2,1,0:T(8,128)(2,1)S(1)}, u32[]{:S(2)}, u32[]{:S(2)}) collective-permute-start(bf16[2,9,32,128]{3,2,1,0:T(8,128)(2,1)S(1)} %collective-permute-done.36.refs_5_), channel_id=1, source_target_pairs={{0,1},{1,0},{2,3},{3,2},{4,5},{5,4},{6,7},{7,6},{8,9},{9,8},{10,11... | collective-permute-start | bytes 442376 | tf_op jit(solution)/shard_map/ppermute | solution.py:223
  103.3 3.5 %collective-permute-start.44 = (bf16[2,9,32,128]{3,2,1,0:T(8,128)(2,1)S(1)}, bf16[2,9,32,128]{3,2,1,0:T(8,128)(2,1)S(1)}, u32[]{:S(2)}, u32[]{:S(2)}) collective-permute-start(bf16[2,9,32,128]{3,2,1,0:T(8,128)(2,1)S(1)} %collective-permute-done.35.refs_6_), channel_id=1, source_target_pairs={{0,1},{1,0},{2,3},{3,2},{4,5},{5,4},{6,7},{7,6},{8,9},{9,8},{10,11... | collective-permute-start | bytes 442376 | tf_op jit(solution)/shard_map/ppermute | solution.py:223
  106.8 1.4 collective-permute-start.45
  113.5 2.1 %collective-permute-start.47 = (bf16[4,2,9,32,128]{4,3,2,1,0:T(8,128)(2,1)S(1)}, bf16[4,2,9,32,128]{4,3,2,1,0:T(8,128)(2,1)S(1)}, u32[]{:S(2)}, u32[]{:S(2)}) collective-permute-start(bf16[4,2,9,32,128]{4,3,2,1,0:T(8,128)(2,1)S(1)} %get-tuple-element.121), channel_id=1, source_target_pairs={{0,1},{1,0},{2,3},{3,2},{4,5},{5,4},{6,7},{7,6},{8,9},{9,8},{10,11... | collective-permute-start | bytes 1769480 | tf_op jit(solution)/shard_map/ppermute | solution.py:223
  113.8 10.4 %collective-permute-start.46 = (bf16[4,2,9,32,128]{4,3,2,1,0:T(8,128)(2,1)S(1)}, bf16[4,2,9,32,128]{4,3,2,1,0:T(8,128)(2,1)S(1)}, u32[]{:S(2)}, u32[]{:S(2)}) collective-permute-start(bf16[4,2,9,32,128]{4,3,2,1,0:T(8,128)(2,1)S(1)} %get-tuple-element.119), channel_id=1, source_target_pairs={{0,1},{1,0},{2,3},{3,2},{4,5},{5,4},{6,7},{7,6},{8,9},{9,8},{10,11... | collective-permute-start | bytes 1769480 | tf_op jit(solution)/shard_map/ppermute | solution.py:223
  115.7 6.0 %collective-permute-start.48 = (bf16[2,9,32,128]{3,2,1,0:T(8,128)(2,1)S(1)}, bf16[2,9,32,128]{3,2,1,0:T(8,128)(2,1)S(1)}, u32[]{:S(2)}, u32[]{:S(2)}) collective-permute-start(bf16[2,9,32,128]{3,2,1,0:T(8,128)(2,1)S(1)} %get-tuple-element.122), channel_id=1, source_target_pairs={{0,8},{1,9},{2,10},{3,11},{4,12},{5,13},{6,14},{7,15},{8,0},{9,1},... | collective-permute-start | bytes 442376 | tf_op jit(solution)/shard_map/ppermute | solution.py:220
  116.7 5.6 %collective-permute-start.49 = (bf16[2,9,32,128]{3,2,1,0:T(8,128)(2,1)S(1)}, bf16[2,9,32,128]{3,2,1,0:T(8,128)(2,1)S(1)}, u32[]{:S(2)}, u32[]{:S(2)}) collective-permute-start(bf16[2,9,32,128]{3,2,1,0:T(8,128)(2,1)S(1)} %get-tuple-element.123), channel_id=1, source_target_pairs={{0,4},{1,5},{2,6},{3,7},{4,0},{5,1},{6,2},{7,3},{8,12},{9,13},{10,... | collective-permute-start | bytes 442376 | tf_op jit(solution)/shard_map/ppermute | solution.py:220
  117.1 5.3 %collective-permute-start.50 = (bf16[2,9,32,128]{3,2,1,0:T(8,128)(2,1)S(1)}, bf16[2,9,32,128]{3,2,1,0:T(8,128)(2,1)S(1)}, u32[]{:S(2)}, u32[]{:S(2)}) collective-permute-start(bf16[2,9,32,128]{3,2,1,0:T(8,128)(2,1)S(1)} %get-tuple-element.124), channel_id=1, source_target_pairs={{0,2},{1,3},{2,0},{3,1},{4,6},{5,7},{6,4},{7,5},{8,10},{9,11},{10,... | collective-permute-start | bytes 442376 | tf_op jit(solution)/shard_map/ppermute | solution.py:220
  122.5 6.3 %collective-permute-start.51 = (bf16[2,9,32,128]{3,2,1,0:T(8,128)(2,1)S(1)}, bf16[2,9,32,128]{3,2,1,0:T(8,128)(2,1)S(1)}, u32[]{:S(2)}, u32[]{:S(2)}) collective-permute-start(bf16[2,9,32,128]{3,2,1,0:T(8,128)(2,1)S(1)} %add_convert_fusion), channel_id=1, source_target_pairs={{0,4},{1,5},{2,6},{3,7},{4,0},{5,1},{6,2},{7,3},{8,12},{9,13},{10,... | collective-permute-start | bytes 442376 | tf_op jit(solution)/shard_map/ppermute | solution.py:220
  124.3 6.0 %collective-permute-start.53 = (bf16[2,9,32,128]{3,2,1,0:T(8,128)(2,1)S(1)}, bf16[2,9,32,128]{3,2,1,0:T(8,128)(2,1)S(1)}, u32[]{:S(2)}, u32[]{:S(2)}) collective-permute-start(bf16[2,9,32,128]{3,2,1,0:T(8,128)(2,1)S(1)} %get-tuple-element.130), channel_id=1, source_target_pairs={{0,4},{1,5},{2,6},{3,7},{4,0},{5,1},{6,2},{7,3},{8,12},{9,13},{10,... | collective-permute-start | bytes 442376 | tf_op jit(solution)/shard_map/ppermute | solution.py:220
  124.8 5.6 %collective-permute-start.54 = (bf16[2,9,32,128]{3,2,1,0:T(8,128)(2,1)S(1)}, bf16[2,9,32,128]{3,2,1,0:T(8,128)(2,1)S(1)}, u32[]{:S(2)}, u32[]{:S(2)}) collective-permute-start(bf16[2,9,32,128]{3,2,1,0:T(8,128)(2,1)S(1)} %get-tuple-element.131), channel_id=1, source_target_pairs={{0,8},{1,9},{2,10},{3,11},{4,12},{5,13},{6,14},{7,15},{8,0},{9,1},... | collective-permute-start | bytes 442376 | tf_op jit(solution)/shard_map/ppermute | solution.py:220
  128.8 5.2 %collective-permute-start.52 = (bf16[2,9,32,128]{3,2,1,0:T(8,128)(2,1)S(1)}, bf16[2,9,32,128]{3,2,1,0:T(8,128)(2,1)S(1)}, u32[]{:S(2)}, u32[]{:S(2)}) collective-permute-start(bf16[2,9,32,128]{3,2,1,0:T(8,128)(2,1)S(1)} %shard_map.109), channel_id=1, source_target_pairs={{0,2},{1,3},{2,0},{3,1},{4,6},{5,7},{6,4},{7,5},{8,10},{9,11},{10,... | collective-permute-start | bytes 442376 | tf_op jit(solution)/shard_map/ppermute | solution.py:220
  134.1 6.1 %collective-permute-start.55 = (bf16[9,32,128]{2,1,0:T(8,128)(2,1)S(1)}, bf16[9,32,128]{2,1,0:T(8,128)(2,1)S(1)}, u32[]{:S(2)}, u32[]{:S(2)}) collective-permute-start(bf16[9,32,128]{2,1,0:T(8,128)(2,1)S(1)} %get-tuple-element.133), channel_id=1, source_target_pairs={{0,16},{1,17},{2,18},{3,19},{4,20},{5,21},{6,22},{7,23},{8,24},{9,... | collective-permute-start | bytes 221192 | tf_op jit(solution)/shard_map/ppermute | solution.py:217
  (6 other events, 4.4 us)

commit v7 on v6

--- a/solution.py
+++ b/solution.py
@@ -216,8 +216,11 @@
     def swap_far(part, shift):
         return lax.ppermute(part, "clu", [(d, (d + shift * cube) % devices) for d in range(devices)])
 
-    def swap(part, chip):
-        return lax.ppermute(part, "clu", [(d, d ^ chip * cores) for d in range(devices)])
+    def swap(part, direction):
+        turned = direction << 1 & 7 | direction >> 2
+        return lax.ppermute(
+            part, "clu", [(d, d ^ (turned if d % cores else direction) * cores) for d in range(devices)]
+        )
 
     def swap_cores(part):
         return lax.ppermute(part, "clu", [(d, d ^ 1) for d in range(devices)])
@@ -228,6 +231,7 @@
         device = cluster // clusters
         core = (device ^ me) % cores
         chip = ((device ^ me) // cores) % chips
+        chip = jnp.where(device % cores == 0, chip, chip >> 1 | (chip & 1) << 2)
         away = (sign * (device // cube - me // cube)) % far
         return ((core * chips + chip) * far + away) * clusters + cluster % clusters
 
@@ -319,20 +323,20 @@
     core = me % cores
     barrier = lax.optimization_barrier
 
+    halo_pairs = [(d, d + cores) for d in range(1, devices - cores, cores)]
+    halo_pairs += [(d, d - cores) for d in range(cores, devices, cores)]
+
     def halo(field_in):
         head, tail = field_in[:1], field_in[leaves - 1 :]
         inner = swap_cores(jnp.where(core == 0, tail, head))
-        pairs = [(d, d + 1) for d in range(1, devices - 1, 2)]
-        outer = lax.ppermute(
-            jnp.where(core == 0, head, tail), "clu", pairs + [(b, a) for a, b in pairs]
-        )
-        return inner, outer
+        return inner, lax.ppermute(jnp.where(core == 0, head, tail), "clu", halo_pairs)
 
     def apply_matrix(field_in, coeffs, with_coeffs):
         away = [swap_far(coeffs, s) for s in range(1, far)]
         away, inner, outer = barrier((away, *halo(field_in)))
         got = {0: jnp.stack([coeffs] + away)}
-        got[x], got[y], got[z] = barrier((swap(got[0], x), swap(got[0], y), swap(got[0], z)))
+        outer = swap_cores(outer)
+        got[x], got[y], got[z], outer = barrier((swap(got[0], x), swap(got[0], y), swap(got[0], z), outer))
         near_sum = near(field_in, near_field)
         got[x | y], got[y | z], got[z | x], near_sum = barrier(
             (swap(got[x], y), swap(got[y], z), swap(got[z], x), near_sum)

time: 143 us -> 142 us (level)
  waiting for transfers between devices: 55.5 us -> 49.9 us
  starting transfers between devices: 50.9 us -> 55.1 us
    ppermute x30, starting transfers between devices: 33.6 us -> 43.1 us  [the longest x28 40.5 us: swap(): lax.ppermute(part, 'clu', [(d, d ^ (turned if d % cores else direction) *...]
    ppermute x30, waiting for transfers between devices: 40.3 us -> 31.9 us  [the longest x28 24.7 us: swap(): lax.ppermute(part, 'clu', [(d, d ^ (turned if d % cores else direction) *...]
    ppermute x22 -> x24, starting transfers between devices: 9.68 us -> 6.7 us  [swap_cores(): return lax.ppermute(part, 'clu', [(d, d ^ 1) for d in range(devices)])]
    ppermute x4, starting transfers between devices: 7.58 us -> 5.29 us  [swap_far(): lax.ppermute(part, 'clu', [(d, (d + shift * cube) % devices) for d in ran...]
    ppermute x4, waiting for transfers between devices: 8.52 us -> 10 us  [swap_far(): lax.ppermute(part, 'clu', [(d, (d + shift * cube) % devices) for d in ran...]
    ppermute x22 -> x24, waiting for transfers between devices: 6.67 us -> 7.96 us  [swap_cores(): return lax.ppermute(part, 'clu', [(d, d ^ 1) for d in range(devices)])]
  transfers between devices with their start and end apart: 56 -> 58, of which waited for: 34 -> 27; matrix products, arithmetic and copies ran while one was open for 4% -> 5% of each run, Pallas kernels for 2% -> 2%
where the time goes in v7:
time: 142 us; the launch traced here: 141 us
  starting transfers between devices  55.1 us (39%)
  waiting for transfers between devices  49.9 us (35%)
  Pallas kernels  21.9 us (15%)
  local copies, waits for them, and re-layouts  11.2 us (8%)
  other arithmetic  2.53 us (2%)
    ppermute x28, starting transfers between devices, swap(): lax.ppermute(part, 'clu', [(d, d ^ (turned if d % cores else direction) *...  40.5 us
    ppermute x28, waiting for transfers between devices, swap(): lax.ppermute(part, 'clu', [(d, d ^ (turned if d % cores else direction) *...  24.7 us
    pallas_call x2, Pallas kernels, apply_matrix(): couple(source_rows, target_rows, coupling, *[got[chip] for chip in range(...  11.7 us
    unnamed x29, local copies, waits for them, and re-layouts  11.2 us
    ppermute x4, waiting for transfers between devices, swap_far(): lax.ppermute(part, 'clu', [(d, (d + shift * cube) % devices) for d in ran...  10 us
    ppermute x24, waiting for transfers between devices, swap_cores(): return lax.ppermute(part, 'clu', [(d, d ^ 1) for d in range(devices)])  7.96 us
    ppermute x2, waiting for transfers between devices, halo(): lax.ppermute(jnp.where(core == 0, head, tail), 'clu', halo_pairs)  7.14 us
    ppermute x24, starting transfers between devices, swap_cores(): return lax.ppermute(part, 'clu', [(d, d ^ 1) for d in range(devices)])  6.7 us
  transfers between devices with their start and end apart: 58, of which 27 were waited for; matrix products, arithmetic and copies ran while one was open for 5% of the time, Pallas kernels for 2%

profile of v7, /device:TPU:0, one launch (start us, length us, event | category | flops | bytes accessed | tf_op | source)
XLA Modules:
  0.0 141.4 jit_solution(14557843200562127445)
XLA Ops:
  0.6 2.9 %shard_map.95 = bf16[9,32,128]{2,1,0:T(8,128)(2,1)} custom-call(s32[12]{0:T(128)} %ranks_ref.5, bf16[8,32,256]{2,1,0:T(8,128)(2,1)} %v_ref.1, bf16[8,96,256]{2,1,0:T(8,128)(2,1)} %basis_ref.3, bf16[8,96,96]{2,1,0:T(8,128)(2,1)} %transfer_ref.3), custom_call_target="tpu_custom_call" | custom-call | tf_op jit(solution)/shard_map/pallas_call | solution.py:244
  3.5 4.1 %collective-permute-start = (bf16[9,32,128]{2,1,0:T(8,128)(2,1)}, bf16[9,32,128]{2,1,0:T(8,128)(2,1)S(1)}, u32[]{:S(2)}, u32[]{:S(2)}) collective-permute-start(bf16[9,32,128]{2,1,0:T(8,128)(2,1)} %shard_map.95), channel_id=1, source_target_pairs={{0,16},{1,17},{2,18},{3,19},{4,20},{5,21},{6,22},{7,23},{8,24},{9,... | collective-permute-start | bytes 221192 | tf_op jit(solution)/shard_map/ppermute | solution.py:217
  7.6 0.7 broadcast_select_fusion.2
  8.4 1.3 collective-permute-start.2
  9.7 1.4 %collective-permute-start.1 = (bf16[1,32,256]{2,1,0:T(8,128)(2,1)S(1)}, bf16[1,32,256]{2,1,0:T(8,128)(2,1)S(1)}, u32[]{:S(2)}, u32[]{:S(2)}) collective-permute-start(bf16[1,32,256]{2,1,0:T(8,128)(2,1)S(1)} %get-tuple-element.141), channel_id=1, source_target_pairs={{0,1},{1,0},{2,3},{3,2},{4,5},{5,4},{6,7},{7,6},{8,9},{9,8},{10,11... | collective-permute-start | bytes 49160 | tf_op jit(solution)/shard_map/ppermute | solution.py:226
  11.1 2.9 %collective-permute-done.2 = bf16[1,32,256]{2,1,0:T(8,128)(2,1)S(1)} collective-permute-done((bf16[1,32,256]{2,1,0:T(8,128)(2,1)S(1)}, bf16[1,32,256]{2,1,0:T(8,128)(2,1)S(1)}, u32[]{:S(2)}, u32[]{:S(2)}) %collective-permute-start.2) | collective-permute-done | bytes 16416 | tf_op jit(solution)/shard_map/ppermute | solution.py:332
  14.0 0.6 copy-done.7
  14.6 0.9 pad_maximum_fusion.refs_0_
  15.5 1.7 %collective-permute-start.5 = (bf16[2,9,32,128]{3,2,1,0:T(8,128)(2,1)S(1)}, bf16[2,9,32,128]{3,2,1,0:T(8,128)(2,1)}, u32[]{:S(2)}, u32[]{:S(2)}) collective-permute-start(bf16[2,9,32,128]{3,2,1,0:T(8,128)(2,1)S(1)} %pad_maximum_fusion.refs_0_), channel_id=1, source_target_pairs={{0,8},{1,3},{2,10},{3,1},{4,12},{5,7},{6,14},{7,5},{8,0},{9,11},{1... | collective-permute-start | bytes 442376 | tf_op jit(solution)/shard_map/ppermute | solution.py:221
  17.2 1.5 %collective-permute-start.4 = (bf16[2,9,32,128]{3,2,1,0:T(8,128)(2,1)S(1)}, bf16[2,9,32,128]{3,2,1,0:T(8,128)(2,1)}, u32[]{:S(2)}, u32[]{:S(2)}) collective-permute-start(bf16[2,9,32,128]{3,2,1,0:T(8,128)(2,1)S(1)} %pad_maximum_fusion.refs_0_), channel_id=1, source_target_pairs={{0,4},{1,9},{2,6},{3,11},{4,0},{5,13},{6,2},{7,15},{8,12},{9,1},{1... | collective-permute-start | bytes 442376 | tf_op jit(solution)/shard_map/ppermute | solution.py:221
  18.7 3.3 %collective-permute-start.3 = (bf16[2,9,32,128]{3,2,1,0:T(8,128)(2,1)S(1)}, bf16[2,9,32,128]{3,2,1,0:T(8,128)(2,1)}, u32[]{:S(2)}, u32[]{:S(2)}) collective-permute-start(bf16[2,9,32,128]{3,2,1,0:T(8,128)(2,1)S(1)} %pad_maximum_fusion.refs_0_), channel_id=1, source_target_pairs={{0,2},{1,5},{2,0},{3,7},{4,6},{5,1},{6,4},{7,3},{8,10},{9,13},{10,... | collective-permute-start | bytes 442376 | tf_op jit(solution)/shard_map/ppermute | solution.py:221
  22.0 1.2 collective-permute-done.6.outer_ref
  23.1 0.6 copy-done.9
  23.8 1.4 %collective-permute-done.3.refs_1_ = bf16[2,9,32,128]{3,2,1,0:T(8,128)(2,1)} collective-permute-done((bf16[2,9,32,128]{3,2,1,0:T(8,128)(2,1)S(1)}, bf16[2,9,32,128]{3,2,1,0:T(8,128)(2,1)}, u32[]{:S(2)}, u32[]{:S(2)}) %collective-permute-start.3) | collective-permute-done | bytes 147488 | tf_op jit(solution)/shard_map/ppermute | solution.py:221
  25.6 2.0 %collective-permute-start.9 = (bf16[2,9,32,128]{3,2,1,0:T(8,128)(2,1)}, bf16[2,9,32,128]{3,2,1,0:T(8,128)(2,1)}, u32[]{:S(2)}, u32[]{:S(2)}) collective-permute-start(bf16[2,9,32,128]{3,2,1,0:T(8,128)(2,1)} %collective-permute-done.5.refs_4_), channel_id=1, source_target_pairs={{0,2},{1,5},{2,0},{3,7},{4,6},{5,1},{6,4},{7,3},{8,10},{9,13},{10,... | collective-permute-start | bytes 442376 | tf_op jit(solution)/shard_map/ppermute | solution.py:221
  27.7 1.9 %copy-done = bf16[8,3,256,256]{3,2,1,0:T(8,128)(2,1)S(1)} copy-done((bf16[8,3,256,256]{3,2,1,0:T(8,128)(2,1)S(1)}, bf16[8,3,256,256]{3,2,1,0:T(8,128)(2,1)}, u32[]{:S(2)}) %copy-start) | copy-done | bytes 3145752
  29.6 0.9 copy-done.5
  30.5 0.6 shard_map.96.near_ref
  32.1 1.6 %collective-permute-start.10 = (bf16[2,9,32,128]{3,2,1,0:T(8,128)(2,1)}, bf16[2,9,32,128]{3,2,1,0:T(8,128)(2,1)}, u32[]{:S(2)}, u32[]{:S(2)}) collective-permute-start(bf16[2,9,32,128]{3,2,1,0:T(8,128)(2,1)} %collective-permute-done.7.refs_3_), channel_id=1, source_target_pairs={{0,8},{1,3},{2,10},{3,1},{4,12},{5,7},{6,14},{7,5},{8,0},{9,11},{1... | collective-permute-start | bytes 442376 | tf_op jit(solution)/shard_map/ppermute | solution.py:221
  33.7 4.8 %copy.10.coupling_ref = bf16[128,96,96]{2,1,0:T(8,128)(2,1)} copy(bf16[128,96,96]{0,2,1:T(8,128)(2,1)} %param.12) | data formatting | bytes 4718592 | tf_op args[4]
  38.5 0.7 copy-done.8
  39.2 0.7 copy-done.10
  41.2 0.7 collective-permute-done.16.refs_13_
  42.5 6.3 %shard_map.98 = (bf16[4,2,9,32,128]{4,3,2,1,0:T(8,128)(2,1)S(1)}, bf16[4,2,9,32,128]{4,3,2,1,0:T(8,128)(2,1)S(1)}, bf16[4,2,9,32,128]{4,3,2,1,0:T(8,128)(2,1)S(1)}, bf16[4,2,9,32,128]{4,3,2,1,0:T(8,128)(2,1)S(1)}) custom-call(s32[128]{0:T(128)S(1)} %get-tuple-element.142.source_ref, s32[128]{0:T(128)S(1)} %get-tuple-element.143.target_ref, ...), custom_call_target="tpu_custom_call" | custom-call | flops 75497472 | bytes 10485760 | tf_op jit(solution)/shard_map/pallas_call | solution.py:349
  49.4 1.5 %collective-permute-done.20.swap_ref = bf16[4,2,9,32,128]{4,3,2,1,0:T(8,128)(2,1)S(1)} collective-permute-done((bf16[4,2,9,32,128]{4,3,2,1,0:T(8,128)(2,1)S(1)}, bf16[4,2,9,32,128]{4,3,2,1,0:T(8,128)(2,1)S(1)}, u32[]{:S(2)}, u32[]{:S(2)}) %collective-permute-start.20) | collective-permute-done | bytes 589856 | tf_op jit(solution)/shard_map/ppermute | solution.py:226
  51.5 2.0 %collective-permute-start.22 = (bf16[2,9,32,128]{3,2,1,0:T(8,128)(2,1)S(1)}, bf16[2,9,32,128]{3,2,1,0:T(8,128)(2,1)S(1)}, u32[]{:S(2)}, u32[]{:S(2)}) collective-permute-start(bf16[2,9,32,128]{3,2,1,0:T(8,128)(2,1)S(1)} %get-tuple-element.92), channel_id=1, source_target_pairs={{0,4},{1,9},{2,6},{3,11},{4,0},{5,13},{6,2},{7,15},{8,12},{9,1},{1... | collective-permute-start | bytes 442376 | tf_op jit(solution)/shard_map/ppermute | solution.py:221
  53.6 1.2 collective-permute-start.23
  54.7 3.0 %collective-permute-done.21 = bf16[2,9,32,128]{3,2,1,0:T(8,128)(2,1)S(1)} collective-permute-done((bf16[2,9,32,128]{3,2,1,0:T(8,128)(2,1)S(1)}, bf16[2,9,32,128]{3,2,1,0:T(8,128)(2,1)S(1)}, u32[]{:S(2)}, u32[]{:S(2)}) %collective-permute-start.21) | collective-permute-done | bytes 147488 | tf_op jit(solution)/shard_map/ppermute | solution.py:221
  58.7 1.5 %collective-permute-start.24 = (bf16[2,9,32,128]{3,2,1,0:T(8,128)(2,1)S(1)}, bf16[2,9,32,128]{3,2,1,0:T(8,128)(2,1)S(1)}, u32[]{:S(2)}, u32[]{:S(2)}) collective-permute-start(bf16[2,9,32,128]{3,2,1,0:T(8,128)(2,1)S(1)} %add_convert_fusion.1), channel_id=1, source_target_pairs={{0,4},{1,9},{2,6},{3,11},{4,0},{5,13},{6,2},{7,15},{8,12},{9,1},{1... | collective-permute-start | bytes 442376 | tf_op jit(solution)/shard_map/ppermute | solution.py:221
  60.4 0.7 collective-permute-start.26
  61.1 1.6 %collective-permute-start.27 = (bf16[2,9,32,128]{3,2,1,0:T(8,128)(2,1)S(1)}, bf16[2,9,32,128]{3,2,1,0:T(8,128)(2,1)S(1)}, u32[]{:S(2)}, u32[]{:S(2)}) collective-permute-start(bf16[2,9,32,128]{3,2,1,0:T(8,128)(2,1)S(1)} %get-tuple-element.100), channel_id=1, source_target_pairs={{0,8},{1,3},{2,10},{3,1},{4,12},{5,7},{6,14},{7,5},{8,0},{9,11},{1... | collective-permute-start | bytes 442376 | tf_op jit(solution)/shard_map/ppermute | solution.py:221
  62.6 1.3 collective-permute-done.24.x_ref
  64.0 1.2 collective-permute-start.25
  66.2 3.0 %collective-permute-done.25.x_ref = bf16[2,9,32,128]{3,2,1,0:T(8,128)(2,1)S(1)} collective-permute-done((bf16[2,9,32,128]{3,2,1,0:T(8,128)(2,1)S(1)}, bf16[2,9,32,128]{3,2,1,0:T(8,128)(2,1)S(1)}, u32[]{:S(2)}, u32[]{:S(2)}) %collective-permute-start.25) | collective-permute-done | bytes 147488 | tf_op jit(solution)/shard_map/ppermute | solution.py:221
  69.7 4.9 %collective-permute-done.28.rest_0_ = bf16[9,32,128]{2,1,0:T(8,128)(2,1)S(1)} collective-permute-done((bf16[9,32,128]{2,1,0:T(8,128)(2,1)S(1)}, bf16[9,32,128]{2,1,0:T(8,128)(2,1)S(1)}, u32[]{:S(2)}, u32[]{:S(2)}) %collective-permute-start.28) | collective-permute-done | bytes 73760 | tf_op jit(solution)/shard_map/ppermute | solution.py:217
  74.6 2.5 %shard_map.103 = (bf16[8,32,256]{2,1,0:T(8,128)(2,1)}, bf16[9,32,128]{2,1,0:T(8,128)(2,1)S(1)}) custom-call(s32[12]{0:T(128)S(1)} %copy-done.11, f32[8,32,256]{2,1,0:T(8,128)S(1)} %shard_map.96.near_ref, f32[2,32,256]{2,1,0:T(8,128)S(1)} %shard_map.97.edge_ref, bf16[8,96,256]{2,1,0:T(8,128)(2,1)S(1)} %copy-done.3, bf16[8,96,96]{2,1,0:T(8,128)(2,1)S(1)} %copy-done.4, ...), custom_call_target="tpu_custom_call" | custom-call | tf_op jit(solution)/shard_map/pallas_call | solution.py:365
  77.6 0.7 broadcast_select_fusion
  78.3 1.3 collective-permute-start.31
  79.7 4.3 %collective-permute-done.31 = bf16[1,32,256]{2,1,0:T(8,128)(2,1)S(1)} collective-permute-done((bf16[1,32,256]{2,1,0:T(8,128)(2,1)S(1)}, bf16[1,32,256]{2,1,0:T(8,128)(2,1)S(1)}, u32[]{:S(2)}, u32[]{:S(2)}) %collective-permute-start.31) | collective-permute-done | bytes 16416 | tf_op jit(solution)/shard_map/ppermute | solution.py:332
  84.0 2.0 %collective-permute-start.34 = (bf16[2,9,32,128]{3,2,1,0:T(8,128)(2,1)S(1)}, bf16[2,9,32,128]{3,2,1,0:T(8,128)(2,1)S(1)}, u32[]{:S(2)}, u32[]{:S(2)}) collective-permute-start(bf16[2,9,32,128]{3,2,1,0:T(8,128)(2,1)S(1)} %pad_maximum_fusion.1.refs_0_), channel_id=1, source_target_pairs={{0,8},{1,3},{2,10},{3,1},{4,12},{5,7},{6,14},{7,5},{8,0},{9,11},{1... | collective-permute-start | bytes 442376 | tf_op jit(solution)/shard_map/ppermute | solution.py:221
  86.0 1.4 collective-permute-start.33
  87.3 2.9 %collective-permute-start.32 = (bf16[2,9,32,128]{3,2,1,0:T(8,128)(2,1)S(1)}, bf16[2,9,32,128]{3,2,1,0:T(8,128)(2,1)S(1)}, u32[]{:S(2)}, u32[]{:S(2)}) collective-permute-start(bf16[2,9,32,128]{3,2,1,0:T(8,128)(2,1)S(1)} %pad_maximum_fusion.1.refs_0_), channel_id=1, source_target_pairs={{0,2},{1,5},{2,0},{3,7},{4,6},{5,1},{6,4},{7,3},{8,10},{9,13},{10,... | collective-permute-start | bytes 442376 | tf_op jit(solution)/shard_map/ppermute | solution.py:221
  90.3 1.2 collective-permute-done.35.outer_ref
  91.4 2.3 %collective-permute-done.32.refs_1_ = bf16[2,9,32,128]{3,2,1,0:T(8,128)(2,1)S(1)} collective-permute-done((bf16[2,9,32,128]{3,2,1,0:T(8,128)(2,1)S(1)}, bf16[2,9,32,128]{3,2,1,0:T(8,128)(2,1)S(1)}, u32[]{:S(2)}, u32[]{:S(2)}) %collective-permute-start.32) | collective-permute-done | bytes 147488 | tf_op jit(solution)/shard_map/ppermute | solution.py:221
  93.7 2.6 %collective-permute-start.38 = (bf16[2,9,32,128]{3,2,1,0:T(8,128)(2,1)S(1)}, bf16[2,9,32,128]{3,2,1,0:T(8,128)(2,1)S(1)}, u32[]{:S(2)}, u32[]{:S(2)}) collective-permute-start(bf16[2,9,32,128]{3,2,1,0:T(8,128)(2,1)S(1)} %collective-permute-done.34.refs_4_), channel_id=1, source_target_pairs={{0,2},{1,5},{2,0},{3,7},{4,6},{5,1},{6,4},{7,3},{8,10},{9,13},{10,... | collective-permute-start | bytes 442376 | tf_op jit(solution)/shard_map/ppermute | solution.py:221
  96.3 0.9 copy-done.6
  97.2 0.6 shard_map.104.near_ref
  99.4 1.9 %collective-permute-start.39 = (bf16[2,9,32,128]{3,2,1,0:T(8,128)(2,1)S(1)}, bf16[2,9,32,128]{3,2,1,0:T(8,128)(2,1)S(1)}, u32[]{:S(2)}, u32[]{:S(2)}) collective-permute-start(bf16[2,9,32,128]{3,2,1,0:T(8,128)(2,1)S(1)} %collective-permute-done.36.refs_3_), channel_id=1, source_target_pairs={{0,8},{1,3},{2,10},{3,1},{4,12},{5,7},{6,14},{7,5},{8,0},{9,11},{1... | collective-permute-start | bytes 442376 | tf_op jit(solution)/shard_map/ppermute | solution.py:221
  102.4 2.2 %collective-permute-done.39.refs_7_ = bf16[2,9,32,128]{3,2,1,0:T(8,128)(2,1)S(1)} collective-permute-done((bf16[2,9,32,128]{3,2,1,0:T(8,128)(2,1)S(1)}, bf16[2,9,32,128]{3,2,1,0:T(8,128)(2,1)S(1)}, u32[]{:S(2)}, u32[]{:S(2)}) %collective-permute-start.39) | collective-permute-done | bytes 147488 | tf_op jit(solution)/shard_map/ppermute | solution.py:221
  104.6 1.3 collective-permute-done.47.refs_15_
  105.9 5.4 %shard_map.106 = (bf16[4,2,9,32,128]{4,3,2,1,0:T(8,128)(2,1)S(1)}, bf16[4,2,9,32,128]{4,3,2,1,0:T(8,128)(2,1)S(1)}, bf16[4,2,9,32,128]{4,3,2,1,0:T(8,128)(2,1)S(1)}, bf16[4,2,9,32,128]{4,3,2,1,0:T(8,128)(2,1)S(1)}) custom-call(s32[128]{0:T(128)S(1)} %get-tuple-element.142.source_ref, s32[128]{0:T(128)S(1)} %get-tuple-element.143.target_ref, ...), custom_call_target="tpu_custom_call" | custom-call | flops 75497472 | bytes 10485760 | tf_op jit(solution)/shard_map/pallas_call | solution.py:349
  111.9 1.5 %collective-permute-done.49.swap_ref = bf16[4,2,9,32,128]{4,3,2,1,0:T(8,128)(2,1)S(1)} collective-permute-done((bf16[4,2,9,32,128]{4,3,2,1,0:T(8,128)(2,1)S(1)}, bf16[4,2,9,32,128]{4,3,2,1,0:T(8,128)(2,1)S(1)}, u32[]{:S(2)}, u32[]{:S(2)}) %collective-permute-start.49) | collective-permute-done | bytes 589856 | tf_op jit(solution)/shard_map/ppermute | solution.py:226
  113.5 2.0 %collective-permute-start.50 = (bf16[2,9,32,128]{3,2,1,0:T(8,128)(2,1)S(1)}, bf16[2,9,32,128]{3,2,1,0:T(8,128)(2,1)S(1)}, u32[]{:S(2)}, u32[]{:S(2)}) collective-permute-start(bf16[2,9,32,128]{3,2,1,0:T(8,128)(2,1)S(1)} %get-tuple-element.126), channel_id=1, source_target_pairs={{0,8},{1,3},{2,10},{3,1},{4,12},{5,7},{6,14},{7,5},{8,0},{9,11},{1... | collective-permute-start | bytes 442376 | tf_op jit(solution)/shard_map/ppermute | solution.py:221
  115.5 2.0 %collective-permute-start.51 = (bf16[2,9,32,128]{3,2,1,0:T(8,128)(2,1)S(1)}, bf16[2,9,32,128]{3,2,1,0:T(8,128)(2,1)S(1)}, u32[]{:S(2)}, u32[]{:S(2)}) collective-permute-start(bf16[2,9,32,128]{3,2,1,0:T(8,128)(2,1)S(1)} %get-tuple-element.127), channel_id=1, source_target_pairs={{0,4},{1,9},{2,6},{3,11},{4,0},{5,13},{6,2},{7,15},{8,12},{9,1},{1... | collective-permute-start | bytes 442376 | tf_op jit(solution)/shard_map/ppermute | solution.py:221
  117.5 2.0 %collective-permute-start.52 = (bf16[2,9,32,128]{3,2,1,0:T(8,128)(2,1)S(1)}, bf16[2,9,32,128]{3,2,1,0:T(8,128)(2,1)S(1)}, u32[]{:S(2)}, u32[]{:S(2)}) collective-permute-start(bf16[2,9,32,128]{3,2,1,0:T(8,128)(2,1)S(1)} %get-tuple-element.128), channel_id=1, source_target_pairs={{0,2},{1,5},{2,0},{3,7},{4,6},{5,1},{6,4},{7,3},{8,10},{9,13},{10,... | collective-permute-start | bytes 442376 | tf_op jit(solution)/shard_map/ppermute | solution.py:221
  119.6 1.8 %collective-permute-done.51.yz_ref = bf16[2,9,32,128]{3,2,1,0:T(8,128)(2,1)S(1)} collective-permute-done((bf16[2,9,32,128]{3,2,1,0:T(8,128)(2,1)S(1)}, bf16[2,9,32,128]{3,2,1,0:T(8,128)(2,1)S(1)}, u32[]{:S(2)}, u32[]{:S(2)}) %collective-permute-start.51) | collective-permute-done | bytes 147488 | tf_op jit(solution)/shard_map/ppermute | solution.py:221
  121.3 1.4 collective-permute-done.52.zx_ref
  122.7 1.0 collective-permute-start.53
  123.9 1.1 collective-permute-start.55
  125.1 2.8 %collective-permute-done.53.x_ref = bf16[2,9,32,128]{3,2,1,0:T(8,128)(2,1)S(1)} collective-permute-done((bf16[2,9,32,128]{3,2,1,0:T(8,128)(2,1)S(1)}, bf16[2,9,32,128]{3,2,1,0:T(8,128)(2,1)S(1)}, u32[]{:S(2)}, u32[]{:S(2)}) %collective-permute-start.53) | collective-permute-done | bytes 147488 | tf_op jit(solution)/shard_map/ppermute | solution.py:221
  128.0 2.2 %collective-permute-start.54 = (bf16[2,9,32,128]{3,2,1,0:T(8,128)(2,1)S(1)}, bf16[2,9,32,128]{3,2,1,0:T(8,128)(2,1)S(1)}, u32[]{:S(2)}, u32[]{:S(2)}) collective-permute-start(bf16[2,9,32,128]{3,2,1,0:T(8,128)(2,1)S(1)} %shard_map.109), channel_id=1, source_target_pairs={{0,2},{1,5},{2,0},{3,7},{4,6},{5,1},{6,4},{7,3},{8,10},{9,13},{10,... | collective-permute-start | bytes 442376 | tf_op jit(solution)/shard_map/ppermute | solution.py:221
  130.3 3.1 %collective-permute-done.54.x_ref = bf16[2,9,32,128]{3,2,1,0:T(8,128)(2,1)S(1)} collective-permute-done((bf16[2,9,32,128]{3,2,1,0:T(8,128)(2,1)S(1)}, bf16[2,9,32,128]{3,2,1,0:T(8,128)(2,1)S(1)}, u32[]{:S(2)}, u32[]{:S(2)}) %collective-permute-start.54) | collective-permute-done | bytes 147488 | tf_op jit(solution)/shard_map/ppermute | solution.py:221
  133.8 5.1 %collective-permute-done.57.rest_0_ = bf16[9,32,128]{2,1,0:T(8,128)(2,1)S(1)} collective-permute-done((bf16[9,32,128]{2,1,0:T(8,128)(2,1)S(1)}, bf16[9,32,128]{2,1,0:T(8,128)(2,1)S(1)}, u32[]{:S(2)}, u32[]{:S(2)}) %collective-permute-start.57) | collective-permute-done | bytes 73760 | tf_op jit(solution)/shard_map/ppermute | solution.py:217
  138.9 2.5 %shard_map.111 = bf16[8,32,256]{2,1,0:T(8,128)(2,1)} custom-call(s32[12]{0:T(128)S(1)} %copy-done.11, f32[8,32,256]{2,1,0:T(8,128)S(1)} %shard_map.104.near_ref, f32[2,32,256]{2,1,0:T(8,128)S(1)} %shard_map.105.edge_ref, bf16[8,96,256]{2,1,0:T(8,128)(2,1)S(1)} %copy-done.3, bf16[8,96,96]{2,1,0:T(8,128)(2,1)S(1)} %copy-done.4, ...), custom_call_target="tpu_custom_call" | custom-call | tf_op jit(solution)/shard_map/pallas_call | solution.py:365
  (105 shorter events, 11.9 us)
Async XLA Ops:
  3.5 11.1 %collective-permute-start = (bf16[9,32,128]{2,1,0:T(8,128)(2,1)}, bf16[9,32,128]{2,1,0:T(8,128)(2,1)S(1)}, u32[]{:S(2)}, u32[]{:S(2)}) collective-permute-start(bf16[9,32,128]{2,1,0:T(8,128)(2,1)} %shard_map.95), channel_id=1, source_target_pairs={{0,16},{1,17},{2,18},{3,19},{4,20},{5,21},{6,22},{7,23},{8,24},{9,... | collective-permute-start | bytes 221192 | tf_op jit(solution)/shard_map/ppermute | solution.py:217
  8.4 5.6 %collective-permute-start.2 = (bf16[1,32,256]{2,1,0:T(8,128)(2,1)S(1)}, bf16[1,32,256]{2,1,0:T(8,128)(2,1)S(1)}, u32[]{:S(2)}, u32[]{:S(2)}) collective-permute-start(bf16[1,32,256]{2,1,0:T(8,128)(2,1)S(1)} %get-tuple-element.140), channel_id=1, source_target_pairs={{1,3},{3,5},{5,7},{7,9},{9,11},{11,13},{13,15},{15,17},{17,19},{19... | collective-permute-start | bytes 49160 | tf_op jit(solution)/shard_map/ppermute | solution.py:332
  9.7 4.3 %collective-permute-start.1 = (bf16[1,32,256]{2,1,0:T(8,128)(2,1)S(1)}, bf16[1,32,256]{2,1,0:T(8,128)(2,1)S(1)}, u32[]{:S(2)}, u32[]{:S(2)}) collective-permute-start(bf16[1,32,256]{2,1,0:T(8,128)(2,1)S(1)} %get-tuple-element.141), channel_id=1, source_target_pairs={{0,1},{1,0},{2,3},{3,2},{4,5},{5,4},{6,7},{7,6},{8,9},{9,8},{10,11... | collective-permute-start | bytes 49160 | tf_op jit(solution)/shard_map/ppermute | solution.py:226
  15.5 8.2 %collective-permute-start.5 = (bf16[2,9,32,128]{3,2,1,0:T(8,128)(2,1)S(1)}, bf16[2,9,32,128]{3,2,1,0:T(8,128)(2,1)}, u32[]{:S(2)}, u32[]{:S(2)}) collective-permute-start(bf16[2,9,32,128]{3,2,1,0:T(8,128)(2,1)S(1)} %pad_maximum_fusion.refs_0_), channel_id=1, source_target_pairs={{0,8},{1,3},{2,10},{3,1},{4,12},{5,7},{6,14},{7,5},{8,0},{9,11},{1... | collective-permute-start | bytes 442376 | tf_op jit(solution)/shard_map/ppermute | solution.py:221
  17.2 6.6 %collective-permute-start.4 = (bf16[2,9,32,128]{3,2,1,0:T(8,128)(2,1)S(1)}, bf16[2,9,32,128]{3,2,1,0:T(8,128)(2,1)}, u32[]{:S(2)}, u32[]{:S(2)}) collective-permute-start(bf16[2,9,32,128]{3,2,1,0:T(8,128)(2,1)S(1)} %pad_maximum_fusion.refs_0_), channel_id=1, source_target_pairs={{0,4},{1,9},{2,6},{3,11},{4,0},{5,13},{6,2},{7,15},{8,12},{9,1},{1... | collective-permute-start | bytes 442376 | tf_op jit(solution)/shard_map/ppermute | solution.py:221
  18.7 6.5 %collective-permute-start.3 = (bf16[2,9,32,128]{3,2,1,0:T(8,128)(2,1)S(1)}, bf16[2,9,32,128]{3,2,1,0:T(8,128)(2,1)}, u32[]{:S(2)}, u32[]{:S(2)}) collective-permute-start(bf16[2,9,32,128]{3,2,1,0:T(8,128)(2,1)S(1)} %pad_maximum_fusion.refs_0_), channel_id=1, source_target_pairs={{0,2},{1,5},{2,0},{3,7},{4,6},{5,1},{6,4},{7,3},{8,10},{9,13},{10,... | collective-permute-start | bytes 442376 | tf_op jit(solution)/shard_map/ppermute | solution.py:221
  22.0 1.2 collective-permute-start.6
  25.2 6.4 %collective-permute-start.7 = (bf16[2,9,32,128]{3,2,1,0:T(8,128)(2,1)}, bf16[2,9,32,128]{3,2,1,0:T(8,128)(2,1)}, u32[]{:S(2)}, u32[]{:S(2)}) collective-permute-start(bf16[2,9,32,128]{3,2,1,0:T(8,128)(2,1)} %collective-permute-done.3.refs_1_), channel_id=1, source_target_pairs={{0,4},{1,9},{2,6},{3,11},{4,0},{5,13},{6,2},{7,15},{8,12},{9,1},{1... | collective-permute-start | bytes 442376 | tf_op jit(solution)/shard_map/ppermute | solution.py:221
  25.2 6.5 %collective-permute-start.8 = (bf16[2,9,32,128]{3,2,1,0:T(8,128)(2,1)}, bf16[2,9,32,128]{3,2,1,0:T(8,128)(2,1)}, u32[]{:S(2)}, u32[]{:S(2)}) collective-permute-start(bf16[2,9,32,128]{3,2,1,0:T(8,128)(2,1)} %collective-permute-done.4.refs_2_), channel_id=1, source_target_pairs={{0,8},{1,3},{2,10},{3,1},{4,12},{5,7},{6,14},{7,5},{8,0},{9,11},{1... | collective-permute-start | bytes 442376 | tf_op jit(solution)/shard_map/ppermute | solution.py:221
  25.6 6.5 %collective-permute-start.9 = (bf16[2,9,32,128]{3,2,1,0:T(8,128)(2,1)}, bf16[2,9,32,128]{3,2,1,0:T(8,128)(2,1)}, u32[]{:S(2)}, u32[]{:S(2)}) collective-permute-start(bf16[2,9,32,128]{3,2,1,0:T(8,128)(2,1)} %collective-permute-done.5.refs_4_), channel_id=1, source_target_pairs={{0,2},{1,5},{2,0},{3,7},{4,6},{5,1},{6,4},{7,3},{8,10},{9,13},{10,... | collective-permute-start | bytes 442376 | tf_op jit(solution)/shard_map/ppermute | solution.py:221
  27.7 1.9 %copy-start = (bf16[8,3,256,256]{3,2,1,0:T(8,128)(2,1)S(1)}, bf16[8,3,256,256]{3,2,1,0:T(8,128)(2,1)}, u32[]{:S(2)}) copy-start(bf16[8,3,256,256]{3,2,1,0:T(8,128)(2,1)} %last_ref.3) | copy-start | bytes 9437188
  31.1 7.4 %copy-start.1 = (bf16[8,3,256,256]{3,2,1,0:T(8,128)(2,1)S(1)}, bf16[8,3,256,256]{3,2,1,0:T(8,128)(2,1)}, u32[]{:S(2)}) copy-start(bf16[8,3,256,256]{3,2,1,0:T(8,128)(2,1)} %last_ref.3) | copy-start | bytes 9437188
  31.1 9.0 %collective-permute-start.11 = (bf16[2,9,32,128]{3,2,1,0:T(8,128)(2,1)S(1)}, bf16[2,9,32,128]{3,2,1,0:T(8,128)(2,1)}, u32[]{:S(2)}, u32[]{:S(2)}) collective-permute-start(bf16[2,9,32,128]{3,2,1,0:T(8,128)(2,1)S(1)} %pad_maximum_fusion.refs_0_), channel_id=1, source_target_pairs={{0,1},{1,0},{2,3},{3,2},{4,5},{5,4},{6,7},{7,6},{8,9},{9,8},{10,11... | collective-permute-start | bytes 442376 | tf_op jit(solution)/shard_map/ppermute | solution.py:226
  31.1 9.1 %collective-permute-start.12 = (bf16[2,9,32,128]{3,2,1,0:T(8,128)(2,1)}, bf16[2,9,32,128]{3,2,1,0:T(8,128)(2,1)}, u32[]{:S(2)}, u32[]{:S(2)}) collective-permute-start(bf16[2,9,32,128]{3,2,1,0:T(8,128)(2,1)} %collective-permute-done.3.refs_1_), channel_id=1, source_target_pairs={{0,1},{1,0},{2,3},{3,2},{4,5},{5,4},{6,7},{7,6},{8,9},{9,8},{10,11... | collective-permute-start | bytes 442376 | tf_op jit(solution)/shard_map/ppermute | solution.py:226
  31.6 9.1 %collective-permute-start.13 = (bf16[2,9,32,128]{3,2,1,0:T(8,128)(2,1)}, bf16[2,9,32,128]{3,2,1,0:T(8,128)(2,1)}, u32[]{:S(2)}, u32[]{:S(2)}) collective-permute-start(bf16[2,9,32,128]{3,2,1,0:T(8,128)(2,1)} %collective-permute-done.4.refs_2_), channel_id=1, source_target_pairs={{0,1},{1,0},{2,3},{3,2},{4,5},{5,4},{6,7},{7,6},{8,9},{9,8},{10,11... | collective-permute-start | bytes 442376 | tf_op jit(solution)/shard_map/ppermute | solution.py:226
  31.7 9.1 %collective-permute-start.14 = (bf16[2,9,32,128]{3,2,1,0:T(8,128)(2,1)}, bf16[2,9,32,128]{3,2,1,0:T(8,128)(2,1)}, u32[]{:S(2)}, u32[]{:S(2)}) collective-permute-start(bf16[2,9,32,128]{3,2,1,0:T(8,128)(2,1)} %collective-permute-done.5.refs_4_), channel_id=1, source_target_pairs={{0,1},{1,0},{2,3},{3,2},{4,5},{5,4},{6,7},{7,6},{8,9},{9,8},{10,11... | collective-permute-start | bytes 442376 | tf_op jit(solution)/shard_map/ppermute | solution.py:226
  32.1 8.6 %collective-permute-start.10 = (bf16[2,9,32,128]{3,2,1,0:T(8,128)(2,1)}, bf16[2,9,32,128]{3,2,1,0:T(8,128)(2,1)}, u32[]{:S(2)}, u32[]{:S(2)}) collective-permute-start(bf16[2,9,32,128]{3,2,1,0:T(8,128)(2,1)} %collective-permute-done.7.refs_3_), channel_id=1, source_target_pairs={{0,8},{1,3},{2,10},{3,1},{4,12},{5,7},{6,14},{7,5},{8,0},{9,11},{1... | collective-permute-start | bytes 442376 | tf_op jit(solution)/shard_map/ppermute | solution.py:221
  39.9 2.5 %copy-start.2 = (bf16[128,96,96]{2,1,0:T(8,128)(2,1)S(1)}, bf16[128,96,96]{2,1,0:T(8,128)(2,1)}, u32[]{:S(2)}) copy-start(bf16[128,96,96]{2,1,0:T(8,128)(2,1)} %copy.10.coupling_ref) | copy-start | bytes 7077892
  40.1 2.2 %collective-permute-start.15 = (bf16[2,9,32,128]{3,2,1,0:T(8,128)(2,1)}, bf16[2,9,32,128]{3,2,1,0:T(8,128)(2,1)S(1)}, u32[]{:S(2)}, u32[]{:S(2)}) collective-permute-start(bf16[2,9,32,128]{3,2,1,0:T(8,128)(2,1)} %collective-permute-done.7.refs_3_), channel_id=1, source_target_pairs={{0,1},{1,0},{2,3},{3,2},{4,5},{5,4},{6,7},{7,6},{8,9},{9,8},{10,11... | collective-permute-start | bytes 442376 | tf_op jit(solution)/shard_map/ppermute | solution.py:226
  40.2 1.8 %collective-permute-start.16 = (bf16[2,9,32,128]{3,2,1,0:T(8,128)(2,1)}, bf16[2,9,32,128]{3,2,1,0:T(8,128)(2,1)S(1)}, u32[]{:S(2)}, u32[]{:S(2)}) collective-permute-start(bf16[2,9,32,128]{3,2,1,0:T(8,128)(2,1)} %collective-permute-done.9.refs_5_), channel_id=1, source_target_pairs={{0,1},{1,0},{2,3},{3,2},{4,5},{5,4},{6,7},{7,6},{8,9},{9,8},{10,11... | collective-permute-start | bytes 442376 | tf_op jit(solution)/shard_map/ppermute | solution.py:226
  40.7 1.6 %collective-permute-start.17 = (bf16[2,9,32,128]{3,2,1,0:T(8,128)(2,1)}, bf16[2,9,32,128]{3,2,1,0:T(8,128)(2,1)S(1)}, u32[]{:S(2)}, u32[]{:S(2)}) collective-permute-start(bf16[2,9,32,128]{3,2,1,0:T(8,128)(2,1)} %collective-permute-done.8.refs_6_), channel_id=1, source_target_pairs={{0,1},{1,0},{2,3},{3,2},{4,5},{5,4},{6,7},{7,6},{8,9},{9,8},{10,11... | collective-permute-start | bytes 442376 | tf_op jit(solution)/shard_map/ppermute | solution.py:226
  40.8 1.7 %collective-permute-start.18 = (bf16[2,9,32,128]{3,2,1,0:T(8,128)(2,1)}, bf16[2,9,32,128]{3,2,1,0:T(8,128)(2,1)S(1)}, u32[]{:S(2)}, u32[]{:S(2)}) collective-permute-start(bf16[2,9,32,128]{3,2,1,0:T(8,128)(2,1)} %collective-permute-done.10.refs_7_), channel_id=1, source_target_pairs={{0,1},{1,0},{2,3},{3,2},{4,5},{5,4},{6,7},{7,6},{8,9},{9,8},{10,11... | collective-permute-start | bytes 442376 | tf_op jit(solution)/shard_map/ppermute | solution.py:226
  48.8 25.8 %copy-start.3 = (bf16[8,96,256]{2,1,0:T(8,128)(2,1)S(1)}, bf16[8,96,256]{2,1,0:T(8,128)(2,1)}, u32[]{:S(2)}) copy-start(bf16[8,96,256]{2,1,0:T(8,128)(2,1)} %basis_ref.3) | copy-start | bytes 1179652
  48.8 25.8 %copy-start.4 = (bf16[8,96,96]{2,1,0:T(8,128)(2,1)S(1)}, bf16[8,96,96]{2,1,0:T(8,128)(2,1)}, u32[]{:S(2)}) copy-start(bf16[8,96,96]{2,1,0:T(8,128)(2,1)} %transfer_ref.3) | copy-start | bytes 442372
  48.8 25.8 %copy-start.11 = (s32[12]{0:T(128)S(1)}, s32[12]{0:T(128)}, u32[]{:S(2)}) copy-start(s32[12]{0:T(128)} %ranks_ref.5) | copy-start | bytes 148
  48.8 2.1 %collective-permute-start.20 = (bf16[4,2,9,32,128]{4,3,2,1,0:T(8,128)(2,1)S(1)}, bf16[4,2,9,32,128]{4,3,2,1,0:T(8,128)(2,1)S(1)}, u32[]{:S(2)}, u32[]{:S(2)}) collective-permute-start(bf16[4,2,9,32,128]{4,3,2,1,0:T(8,128)(2,1)S(1)} %get-tuple-element.90), channel_id=1, source_target_pairs={{0,1},{1,0},{2,3},{3,2},{4,5},{5,4},{6,7},{7,6},{8,9},{9,8},{10,11... | collective-permute-start | bytes 1769480 | tf_op jit(solution)/shard_map/ppermute | solution.py:226
  49.2 11.1 %collective-permute-start.19 = (bf16[4,2,9,32,128]{4,3,2,1,0:T(8,128)(2,1)S(1)}, bf16[4,2,9,32,128]{4,3,2,1,0:T(8,128)(2,1)S(1)}, u32[]{:S(2)}, u32[]{:S(2)}) collective-permute-start(bf16[4,2,9,32,128]{4,3,2,1,0:T(8,128)(2,1)S(1)} %get-tuple-element.88), channel_id=1, source_target_pairs={{0,1},{1,0},{2,3},{3,2},{4,5},{5,4},{6,7},{7,6},{8,9},{9,8},{10,11... | collective-permute-start | bytes 1769480 | tf_op jit(solution)/shard_map/ppermute | solution.py:226
  51.0 6.7 %collective-permute-start.21 = (bf16[2,9,32,128]{3,2,1,0:T(8,128)(2,1)S(1)}, bf16[2,9,32,128]{3,2,1,0:T(8,128)(2,1)S(1)}, u32[]{:S(2)}, u32[]{:S(2)}) collective-permute-start(bf16[2,9,32,128]{3,2,1,0:T(8,128)(2,1)S(1)} %get-tuple-element.91), channel_id=1, source_target_pairs={{0,8},{1,3},{2,10},{3,1},{4,12},{5,7},{6,14},{7,5},{8,0},{9,11},{1... | collective-permute-start | bytes 442376 | tf_op jit(solution)/shard_map/ppermute | solution.py:221
  51.5 6.6 %collective-permute-start.22 = (bf16[2,9,32,128]{3,2,1,0:T(8,128)(2,1)S(1)}, bf16[2,9,32,128]{3,2,1,0:T(8,128)(2,1)S(1)}, u32[]{:S(2)}, u32[]{:S(2)}) collective-permute-start(bf16[2,9,32,128]{3,2,1,0:T(8,128)(2,1)S(1)} %get-tuple-element.92), channel_id=1, source_target_pairs={{0,4},{1,9},{2,6},{3,11},{4,0},{5,13},{6,2},{7,15},{8,12},{9,1},{1... | collective-permute-start | bytes 442376 | tf_op jit(solution)/shard_map/ppermute | solution.py:221
  53.6 5.1 %collective-permute-start.23 = (bf16[2,9,32,128]{3,2,1,0:T(8,128)(2,1)S(1)}, bf16[2,9,32,128]{3,2,1,0:T(8,128)(2,1)S(1)}, u32[]{:S(2)}, u32[]{:S(2)}) collective-permute-start(bf16[2,9,32,128]{3,2,1,0:T(8,128)(2,1)S(1)} %get-tuple-element.93), channel_id=1, source_target_pairs={{0,2},{1,5},{2,0},{3,7},{4,6},{5,1},{6,4},{7,3},{8,10},{9,13},{10,... | collective-permute-start | bytes 442376 | tf_op jit(solution)/shard_map/ppermute | solution.py:221
  58.7 5.2 %collective-permute-start.24 = (bf16[2,9,32,128]{3,2,1,0:T(8,128)(2,1)S(1)}, bf16[2,9,32,128]{3,2,1,0:T(8,128)(2,1)S(1)}, u32[]{:S(2)}, u32[]{:S(2)}) collective-permute-start(bf16[2,9,32,128]{3,2,1,0:T(8,128)(2,1)S(1)} %add_convert_fusion.1), channel_id=1, source_target_pairs={{0,4},{1,9},{2,6},{3,11},{4,0},{5,13},{6,2},{7,15},{8,12},{9,1},{1... | collective-permute-start | bytes 442376 | tf_op jit(solution)/shard_map/ppermute | solution.py:221
  60.4 5.3 %collective-permute-start.26 = (bf16[2,9,32,128]{3,2,1,0:T(8,128)(2,1)S(1)}, bf16[2,9,32,128]{3,2,1,0:T(8,128)(2,1)S(1)}, u32[]{:S(2)}, u32[]{:S(2)}) collective-permute-start(bf16[2,9,32,128]{3,2,1,0:T(8,128)(2,1)S(1)} %get-tuple-element.99), channel_id=1, source_target_pairs={{0,4},{1,9},{2,6},{3,11},{4,0},{5,13},{6,2},{7,15},{8,12},{9,1},{1... | collective-permute-start | bytes 442376 | tf_op jit(solution)/shard_map/ppermute | solution.py:221
  61.1 5.1 %collective-permute-start.27 = (bf16[2,9,32,128]{3,2,1,0:T(8,128)(2,1)S(1)}, bf16[2,9,32,128]{3,2,1,0:T(8,128)(2,1)S(1)}, u32[]{:S(2)}, u32[]{:S(2)}) collective-permute-start(bf16[2,9,32,128]{3,2,1,0:T(8,128)(2,1)S(1)} %get-tuple-element.100), channel_id=1, source_target_pairs={{0,8},{1,3},{2,10},{3,1},{4,12},{5,7},{6,14},{7,5},{8,0},{9,11},{1... | collective-permute-start | bytes 442376 | tf_op jit(solution)/shard_map/ppermute | solution.py:221
  64.0 5.2 %collective-permute-start.25 = (bf16[2,9,32,128]{3,2,1,0:T(8,128)(2,1)S(1)}, bf16[2,9,32,128]{3,2,1,0:T(8,128)(2,1)S(1)}, u32[]{:S(2)}, u32[]{:S(2)}) collective-permute-start(bf16[2,9,32,128]{3,2,1,0:T(8,128)(2,1)S(1)} %shard_map.101), channel_id=1, source_target_pairs={{0,2},{1,5},{2,0},{3,7},{4,6},{5,1},{6,4},{7,3},{8,10},{9,13},{10,... | collective-permute-start | bytes 442376 | tf_op jit(solution)/shard_map/ppermute | solution.py:221
  69.3 5.3 %collective-permute-start.28 = (bf16[9,32,128]{2,1,0:T(8,128)(2,1)S(1)}, bf16[9,32,128]{2,1,0:T(8,128)(2,1)S(1)}, u32[]{:S(2)}, u32[]{:S(2)}) collective-permute-start(bf16[9,32,128]{2,1,0:T(8,128)(2,1)S(1)} %get-tuple-element.102), channel_id=1, source_target_pairs={{0,16},{1,17},{2,18},{3,19},{4,20},{5,21},{6,22},{7,23},{8,24},{9,... | collective-permute-start | bytes 221192 | tf_op jit(solution)/shard_map/ppermute | solution.py:217
  77.1 6.8 %collective-permute-start.29 = (bf16[9,32,128]{2,1,0:T(8,128)(2,1)S(1)}, bf16[9,32,128]{2,1,0:T(8,128)(2,1)S(1)}, u32[]{:S(2)}, u32[]{:S(2)}) collective-permute-start(bf16[9,32,128]{2,1,0:T(8,128)(2,1)S(1)} %get-tuple-element.104), channel_id=1, source_target_pairs={{0,16},{1,17},{2,18},{3,19},{4,20},{5,21},{6,22},{7,23},{8,24},{9,... | collective-permute-start | bytes 221192 | tf_op jit(solution)/shard_map/ppermute | solution.py:217
  78.3 5.6 %collective-permute-start.31 = (bf16[1,32,256]{2,1,0:T(8,128)(2,1)S(1)}, bf16[1,32,256]{2,1,0:T(8,128)(2,1)S(1)}, u32[]{:S(2)}, u32[]{:S(2)}) collective-permute-start(bf16[1,32,256]{2,1,0:T(8,128)(2,1)S(1)} %get-tuple-element.138), channel_id=1, source_target_pairs={{1,3},{3,5},{5,7},{7,9},{9,11},{11,13},{13,15},{15,17},{17,19},{19... | collective-permute-start | bytes 49160 | tf_op jit(solution)/shard_map/ppermute | solution.py:332
  79.6 4.3 %collective-permute-start.30 = (bf16[1,32,256]{2,1,0:T(8,128)(2,1)S(1)}, bf16[1,32,256]{2,1,0:T(8,128)(2,1)S(1)}, u32[]{:S(2)}, u32[]{:S(2)}) collective-permute-start(bf16[1,32,256]{2,1,0:T(8,128)(2,1)S(1)} %get-tuple-element.139), channel_id=1, source_target_pairs={{0,1},{1,0},{2,3},{3,2},{4,5},{5,4},{6,7},{7,6},{8,9},{9,8},{10,11... | collective-permute-start | bytes 49160 | tf_op jit(solution)/shard_map/ppermute | solution.py:226
  84.0 7.5 %collective-permute-start.34 = (bf16[2,9,32,128]{3,2,1,0:T(8,128)(2,1)S(1)}, bf16[2,9,32,128]{3,2,1,0:T(8,128)(2,1)S(1)}, u32[]{:S(2)}, u32[]{:S(2)}) collective-permute-start(bf16[2,9,32,128]{3,2,1,0:T(8,128)(2,1)S(1)} %pad_maximum_fusion.1.refs_0_), channel_id=1, source_target_pairs={{0,8},{1,3},{2,10},{3,1},{4,12},{5,7},{6,14},{7,5},{8,0},{9,11},{1... | collective-permute-start | bytes 442376 | tf_op jit(solution)/shard_map/ppermute | solution.py:221
  86.0 5.5 %collective-permute-start.33 = (bf16[2,9,32,128]{3,2,1,0:T(8,128)(2,1)S(1)}, bf16[2,9,32,128]{3,2,1,0:T(8,128)(2,1)S(1)}, u32[]{:S(2)}, u32[]{:S(2)}) collective-permute-start(bf16[2,9,32,128]{3,2,1,0:T(8,128)(2,1)S(1)} %pad_maximum_fusion.1.refs_0_), channel_id=1, source_target_pairs={{0,4},{1,9},{2,6},{3,11},{4,0},{5,13},{6,2},{7,15},{8,12},{9,1},{1... | collective-permute-start | bytes 442376 | tf_op jit(solution)/shard_map/ppermute | solution.py:221
  87.3 6.4 %collective-permute-start.32 = (bf16[2,9,32,128]{3,2,1,0:T(8,128)(2,1)S(1)}, bf16[2,9,32,128]{3,2,1,0:T(8,128)(2,1)S(1)}, u32[]{:S(2)}, u32[]{:S(2)}) collective-permute-start(bf16[2,9,32,128]{3,2,1,0:T(8,128)(2,1)S(1)} %pad_maximum_fusion.1.refs_0_), channel_id=1, source_target_pairs={{0,2},{1,5},{2,0},{3,7},{4,6},{5,1},{6,4},{7,3},{8,10},{9,13},{10,... | collective-permute-start | bytes 442376 | tf_op jit(solution)/shard_map/ppermute | solution.py:221
  90.3 1.2 collective-permute-start.35
  93.7 5.1 %collective-permute-start.36 = (bf16[2,9,32,128]{3,2,1,0:T(8,128)(2,1)S(1)}, bf16[2,9,32,128]{3,2,1,0:T(8,128)(2,1)S(1)}, u32[]{:S(2)}, u32[]{:S(2)}) collective-permute-start(bf16[2,9,32,128]{3,2,1,0:T(8,128)(2,1)S(1)} %collective-permute-done.32.refs_1_), channel_id=1, source_target_pairs={{0,4},{1,9},{2,6},{3,11},{4,0},{5,13},{6,2},{7,15},{8,12},{9,1},{1... | collective-permute-start | bytes 442376 | tf_op jit(solution)/shard_map/ppermute | solution.py:221
  93.7 5.1 %collective-permute-start.37 = (bf16[2,9,32,128]{3,2,1,0:T(8,128)(2,1)S(1)}, bf16[2,9,32,128]{3,2,1,0:T(8,128)(2,1)S(1)}, u32[]{:S(2)}, u32[]{:S(2)}) collective-permute-start(bf16[2,9,32,128]{3,2,1,0:T(8,128)(2,1)S(1)} %collective-permute-done.33.refs_2_), channel_id=1, source_target_pairs={{0,8},{1,3},{2,10},{3,1},{4,12},{5,7},{6,14},{7,5},{8,0},{9,11},{1... | collective-permute-start | bytes 442376 | tf_op jit(solution)/shard_map/ppermute | solution.py:221
  93.7 5.7 %collective-permute-start.38 = (bf16[2,9,32,128]{3,2,1,0:T(8,128)(2,1)S(1)}, bf16[2,9,32,128]{3,2,1,0:T(8,128)(2,1)S(1)}, u32[]{:S(2)}, u32[]{:S(2)}) collective-permute-start(bf16[2,9,32,128]{3,2,1,0:T(8,128)(2,1)S(1)} %collective-permute-done.34.refs_4_), channel_id=1, source_target_pairs={{0,2},{1,5},{2,0},{3,7},{4,6},{5,1},{6,4},{7,3},{8,10},{9,13},{10,... | collective-permute-start | bytes 442376 | tf_op jit(solution)/shard_map/ppermute | solution.py:221
  97.8 3.7 %collective-permute-start.40 = (bf16[2,9,32,128]{3,2,1,0:T(8,128)(2,1)S(1)}, bf16[2,9,32,128]{3,2,1,0:T(8,128)(2,1)S(1)}, u32[]{:S(2)}, u32[]{:S(2)}) collective-permute-start(bf16[2,9,32,128]{3,2,1,0:T(8,128)(2,1)S(1)} %pad_maximum_fusion.1.refs_0_), channel_id=1, source_target_pairs={{0,1},{1,0},{2,3},{3,2},{4,5},{5,4},{6,7},{7,6},{8,9},{9,8},{10,11... | collective-permute-start | bytes 442376 | tf_op jit(solution)/shard_map/ppermute | solution.py:226
  97.8 4.1 %collective-permute-start.41 = (bf16[2,9,32,128]{3,2,1,0:T(8,128)(2,1)S(1)}, bf16[2,9,32,128]{3,2,1,0:T(8,128)(2,1)S(1)}, u32[]{:S(2)}, u32[]{:S(2)}) collective-permute-start(bf16[2,9,32,128]{3,2,1,0:T(8,128)(2,1)S(1)} %collective-permute-done.32.refs_1_), channel_id=1, source_target_pairs={{0,1},{1,0},{2,3},{3,2},{4,5},{5,4},{6,7},{7,6},{8,9},{9,8},{10,11... | collective-permute-start | bytes 442376 | tf_op jit(solution)/shard_map/ppermute | solution.py:226
  98.8 3.2 %collective-permute-start.42 = (bf16[2,9,32,128]{3,2,1,0:T(8,128)(2,1)S(1)}, bf16[2,9,32,128]{3,2,1,0:T(8,128)(2,1)S(1)}, u32[]{:S(2)}, u32[]{:S(2)}) collective-permute-start(bf16[2,9,32,128]{3,2,1,0:T(8,128)(2,1)S(1)} %collective-permute-done.33.refs_2_), channel_id=1, source_target_pairs={{0,1},{1,0},{2,3},{3,2},{4,5},{5,4},{6,7},{7,6},{8,9},{9,8},{10,11... | collective-permute-start | bytes 442376 | tf_op jit(solution)/shard_map/ppermute | solution.py:226
  98.9 3.5 %collective-permute-start.43 = (bf16[2,9,32,128]{3,2,1,0:T(8,128)(2,1)S(1)}, bf16[2,9,32,128]{3,2,1,0:T(8,128)(2,1)S(1)}, u32[]{:S(2)}, u32[]{:S(2)}) collective-permute-start(bf16[2,9,32,128]{3,2,1,0:T(8,128)(2,1)S(1)} %collective-permute-done.34.refs_4_), channel_id=1, source_target_pairs={{0,1},{1,0},{2,3},{3,2},{4,5},{5,4},{6,7},{7,6},{8,9},{9,8},{10,11... | collective-permute-start | bytes 442376 | tf_op jit(solution)/shard_map/ppermute | solution.py:226
  99.4 5.1 %collective-permute-start.39 = (bf16[2,9,32,128]{3,2,1,0:T(8,128)(2,1)S(1)}, bf16[2,9,32,128]{3,2,1,0:T(8,128)(2,1)S(1)}, u32[]{:S(2)}, u32[]{:S(2)}) collective-permute-start(bf16[2,9,32,128]{3,2,1,0:T(8,128)(2,1)S(1)} %collective-permute-done.36.refs_3_), channel_id=1, source_target_pairs={{0,8},{1,3},{2,10},{3,1},{4,12},{5,7},{6,14},{7,5},{8,0},{9,11},{1... | collective-permute-start | bytes 442376 | tf_op jit(solution)/shard_map/ppermute | solution.py:221
  101.5 3.1 %collective-permute-start.44 = (bf16[2,9,32,128]{3,2,1,0:T(8,128)(2,1)S(1)}, bf16[2,9,32,128]{3,2,1,0:T(8,128)(2,1)S(1)}, u32[]{:S(2)}, u32[]{:S(2)}) collective-permute-start(bf16[2,9,32,128]{3,2,1,0:T(8,128)(2,1)S(1)} %collective-permute-done.36.refs_3_), channel_id=1, source_target_pairs={{0,1},{1,0},{2,3},{3,2},{4,5},{5,4},{6,7},{7,6},{8,9},{9,8},{10,11... | collective-permute-start | bytes 442376 | tf_op jit(solution)/shard_map/ppermute | solution.py:226
  101.9 2.7 %collective-permute-start.45 = (bf16[2,9,32,128]{3,2,1,0:T(8,128)(2,1)S(1)}, bf16[2,9,32,128]{3,2,1,0:T(8,128)(2,1)S(1)}, u32[]{:S(2)}, u32[]{:S(2)}) collective-permute-start(bf16[2,9,32,128]{3,2,1,0:T(8,128)(2,1)S(1)} %collective-permute-done.38.refs_5_), channel_id=1, source_target_pairs={{0,1},{1,0},{2,3},{3,2},{4,5},{5,4},{6,7},{7,6},{8,9},{9,8},{10,11... | collective-permute-start | bytes 442376 | tf_op jit(solution)/shard_map/ppermute | solution.py:226
  102.1 2.5 %collective-permute-start.46 = (bf16[2,9,32,128]{3,2,1,0:T(8,128)(2,1)S(1)}, bf16[2,9,32,128]{3,2,1,0:T(8,128)(2,1)S(1)}, u32[]{:S(2)}, u32[]{:S(2)}) collective-permute-start(bf16[2,9,32,128]{3,2,1,0:T(8,128)(2,1)S(1)} %collective-permute-done.37.refs_6_), channel_id=1, source_target_pairs={{0,1},{1,0},{2,3},{3,2},{4,5},{5,4},{6,7},{7,6},{8,9},{9,8},{10,11... | collective-permute-start | bytes 442376 | tf_op jit(solution)/shard_map/ppermute | solution.py:226
  104.5 1.4 collective-permute-start.47
  111.3 2.1 %collective-permute-start.49 = (bf16[4,2,9,32,128]{4,3,2,1,0:T(8,128)(2,1)S(1)}, bf16[4,2,9,32,128]{4,3,2,1,0:T(8,128)(2,1)S(1)}, u32[]{:S(2)}, u32[]{:S(2)}) collective-permute-start(bf16[4,2,9,32,128]{4,3,2,1,0:T(8,128)(2,1)S(1)} %get-tuple-element.125), channel_id=1, source_target_pairs={{0,1},{1,0},{2,3},{3,2},{4,5},{5,4},{6,7},{7,6},{8,9},{9,8},{10,11... | collective-permute-start | bytes 1769480 | tf_op jit(solution)/shard_map/ppermute | solution.py:226
  111.5 12.3 %collective-permute-start.48 = (bf16[4,2,9,32,128]{4,3,2,1,0:T(8,128)(2,1)S(1)}, bf16[4,2,9,32,128]{4,3,2,1,0:T(8,128)(2,1)S(1)}, u32[]{:S(2)}, u32[]{:S(2)}) collective-permute-start(bf16[4,2,9,32,128]{4,3,2,1,0:T(8,128)(2,1)S(1)} %get-tuple-element.123), channel_id=1, source_target_pairs={{0,1},{1,0},{2,3},{3,2},{4,5},{5,4},{6,7},{7,6},{8,9},{9,8},{10,11... | collective-permute-start | bytes 1769480 | tf_op jit(solution)/shard_map/ppermute | solution.py:226
  113.5 6.1 %collective-permute-start.50 = (bf16[2,9,32,128]{3,2,1,0:T(8,128)(2,1)S(1)}, bf16[2,9,32,128]{3,2,1,0:T(8,128)(2,1)S(1)}, u32[]{:S(2)}, u32[]{:S(2)}) collective-permute-start(bf16[2,9,32,128]{3,2,1,0:T(8,128)(2,1)S(1)} %get-tuple-element.126), channel_id=1, source_target_pairs={{0,8},{1,3},{2,10},{3,1},{4,12},{5,7},{6,14},{7,5},{8,0},{9,11},{1... | collective-permute-start | bytes 442376 | tf_op jit(solution)/shard_map/ppermute | solution.py:221
  115.5 5.8 %collective-permute-start.51 = (bf16[2,9,32,128]{3,2,1,0:T(8,128)(2,1)S(1)}, bf16[2,9,32,128]{3,2,1,0:T(8,128)(2,1)S(1)}, u32[]{:S(2)}, u32[]{:S(2)}) collective-permute-start(bf16[2,9,32,128]{3,2,1,0:T(8,128)(2,1)S(1)} %get-tuple-element.127), channel_id=1, source_target_pairs={{0,4},{1,9},{2,6},{3,11},{4,0},{5,13},{6,2},{7,15},{8,12},{9,1},{1... | collective-permute-start | bytes 442376 | tf_op jit(solution)/shard_map/ppermute | solution.py:221
  117.5 5.2 %collective-permute-start.52 = (bf16[2,9,32,128]{3,2,1,0:T(8,128)(2,1)S(1)}, bf16[2,9,32,128]{3,2,1,0:T(8,128)(2,1)S(1)}, u32[]{:S(2)}, u32[]{:S(2)}) collective-permute-start(bf16[2,9,32,128]{3,2,1,0:T(8,128)(2,1)S(1)} %get-tuple-element.128), channel_id=1, source_target_pairs={{0,2},{1,5},{2,0},{3,7},{4,6},{5,1},{6,4},{7,3},{8,10},{9,13},{10,... | collective-permute-start | bytes 442376 | tf_op jit(solution)/shard_map/ppermute | solution.py:221
  122.7 5.2 %collective-permute-start.53 = (bf16[2,9,32,128]{3,2,1,0:T(8,128)(2,1)S(1)}, bf16[2,9,32,128]{3,2,1,0:T(8,128)(2,1)S(1)}, u32[]{:S(2)}, u32[]{:S(2)}) collective-permute-start(bf16[2,9,32,128]{3,2,1,0:T(8,128)(2,1)S(1)} %add_convert_fusion), channel_id=1, source_target_pairs={{0,4},{1,9},{2,6},{3,11},{4,0},{5,13},{6,2},{7,15},{8,12},{9,1},{1... | collective-permute-start | bytes 442376 | tf_op jit(solution)/shard_map/ppermute | solution.py:221
  123.9 6.3 %collective-permute-start.55 = (bf16[2,9,32,128]{3,2,1,0:T(8,128)(2,1)S(1)}, bf16[2,9,32,128]{3,2,1,0:T(8,128)(2,1)S(1)}, u32[]{:S(2)}, u32[]{:S(2)}) collective-permute-start(bf16[2,9,32,128]{3,2,1,0:T(8,128)(2,1)S(1)} %get-tuple-element.134), channel_id=1, source_target_pairs={{0,4},{1,9},{2,6},{3,11},{4,0},{5,13},{6,2},{7,15},{8,12},{9,1},{1... | collective-permute-start | bytes 442376 | tf_op jit(solution)/shard_map/ppermute | solution.py:221
  125.0 5.2 %collective-permute-start.56 = (bf16[2,9,32,128]{3,2,1,0:T(8,128)(2,1)S(1)}, bf16[2,9,32,128]{3,2,1,0:T(8,128)(2,1)S(1)}, u32[]{:S(2)}, u32[]{:S(2)}) collective-permute-start(bf16[2,9,32,128]{3,2,1,0:T(8,128)(2,1)S(1)} %get-tuple-element.135), channel_id=1, source_target_pairs={{0,8},{1,3},{2,10},{3,1},{4,12},{5,7},{6,14},{7,5},{8,0},{9,11},{1... | collective-permute-start | bytes 442376 | tf_op jit(solution)/shard_map/ppermute | solution.py:221
  128.0 5.4 %collective-permute-start.54 = (bf16[2,9,32,128]{3,2,1,0:T(8,128)(2,1)S(1)}, bf16[2,9,32,128]{3,2,1,0:T(8,128)(2,1)S(1)}, u32[]{:S(2)}, u32[]{:S(2)}) collective-permute-start(bf16[2,9,32,128]{3,2,1,0:T(8,128)(2,1)S(1)} %shard_map.109), channel_id=1, source_target_pairs={{0,2},{1,5},{2,0},{3,7},{4,6},{5,1},{6,4},{7,3},{8,10},{9,13},{10,... | collective-permute-start | bytes 442376 | tf_op jit(solution)/shard_map/ppermute | solution.py:221
  133.4 5.5 %collective-permute-start.57 = (bf16[9,32,128]{2,1,0:T(8,128)(2,1)S(1)}, bf16[9,32,128]{2,1,0:T(8,128)(2,1)S(1)}, u32[]{:S(2)}, u32[]{:S(2)}) collective-permute-start(bf16[9,32,128]{2,1,0:T(8,128)(2,1)S(1)} %get-tuple-element.137), channel_id=1, source_target_pairs={{0,16},{1,17},{2,18},{3,19},{4,20},{5,21},{6,22},{7,23},{8,24},{9,... | collective-permute-start | bytes 221192 | tf_op jit(solution)/shard_map/ppermute | solution.py:217
  (8 other events, 7.0 us)

commit v8 on v7

--- a/solution.py
+++ b/solution.py
@@ -326,35 +326,31 @@
     halo_pairs = [(d, d + cores) for d in range(1, devices - cores, cores)]
     halo_pairs += [(d, d - cores) for d in range(cores, devices, cores)]
 
-    def halo(field_in):
+    def apply_matrix(field_in, coeffs, coupling, with_coeffs):
         head, tail = field_in[:1], field_in[leaves - 1 :]
-        inner = swap_cores(jnp.where(core == 0, tail, head))
-        return inner, lax.ppermute(jnp.where(core == 0, head, tail), "clu", halo_pairs)
-
-    def apply_matrix(field_in, coeffs, with_coeffs):
         away = [swap_far(coeffs, s) for s in range(1, far)]
-        away, inner, outer = barrier((away, *halo(field_in)))
+        away, coupling = barrier((away, coupling))
         got = {0: jnp.stack([coeffs] + away)}
-        outer = swap_cores(outer)
-        got[x], got[y], got[z], outer = barrier((swap(got[0], x), swap(got[0], y), swap(got[0], z), outer))
+        got[x], got[y], got[z] = barrier((swap(got[0], x), swap(got[0], y), swap(got[0], z)))
         near_sum = near(field_in, near_field)
-        got[x | y], got[y | z], got[z | x], near_sum = barrier(
-            (swap(got[x], y), swap(got[y], z), swap(got[z], x), near_sum)
-        )
-        edges = edge(core.reshape(1), inner, outer, near_field, near_field)
-        other = {chip: swap_cores(got[chip]) for chip in (0, x, y, z)}
-        got[x | y | z], edges, other = barrier((swap(got[x | y], z), edges, other))
-        for chip in (x | y, y | z, z | x, x | y | z):
-            other[chip] = swap_cores(got[chip])
-        keep_first, keep, send_first, send = couple(
+        got |= {x | y: swap(got[x], y), y | z: swap(got[y], z), z | x: swap(got[z], x)}
+        got, near_sum = barrier((got, near_sum))
+        other = {chip: swap_cores(got[chip]) for chip in got}
+        got[x | y | z], outer = barrier((swap(got[x | y], z), jnp.where(core == 0, head, tail)))
+        other[x | y | z] = swap_cores(got[x | y | z])
+        outer = lax.ppermute(outer, "clu", halo_pairs)
+        totals = couple(
             source_rows,
             target_rows,
             coupling,
             *[got[chip] for chip in range(chips)],
             *[other[chip] for chip in range(chips)],
         )
+        (keep_first, keep, send_first, send), outer = barrier((totals, outer))
         corner, xy, yz, zx = first_add(keep_first, swap_cores(send_first))
         swapped = swap_cores(send)
+        inner, outer = swap_cores(jnp.where(core == 0, tail, head)), swap_cores(outer)
+        edges = edge(core.reshape(1), inner, outer, near_field, near_field)
         corner, yz, zx = barrier((swap(corner, z), swap(yz, y), swap(zx, x)))
         xy = swap((xy.astype(F32) + corner.astype(F32)).astype(BF), y)
         mine, to_y, to_z = second_add(keep, swapped, yz, zx)
@@ -364,8 +360,16 @@
         terms = [swap_far(part, s + 1) for s, part in enumerate(away)]
         return finish(with_coeffs)(ranks, near_sum, edges, basis, transfer, total, *terms)
 
-    first, second_coeffs = apply_matrix(charges, first_coeffs, True)
-    (second,) = apply_matrix(first, second_coeffs, False)
+    coupling, first_coeffs = barrier((coupling, first_coeffs))
+    coupling = pl.pallas_call(
+        lambda in_ref, out_ref: None,
+        out_shape=shape(coupling.shape, BF),
+        in_specs=[pl.BlockSpec(memory_space=pl.ANY)],
+        out_specs=pl.BlockSpec(memory_space=pl.ANY),
+        input_output_aliases={0: 0},
+    )(coupling)
+    first, second_coeffs = apply_matrix(charges, first_coeffs, coupling, True)
+    (second,) = apply_matrix(first, second_coeffs, coupling, False)
     return (first, second)
 
 

time: 142 us -> 144 us (1.014)
  waiting for transfers between devices: 49.9 us -> 66.5 us
  starting transfers between devices: 55.1 us -> 46.5 us
  local copies, waits for them, and re-layouts: 11.2 us -> 6.56 us
    ppermute x28, waiting for transfers between devices: 24.7 us -> 47.8 us  [swap(): lax.ppermute(part, 'clu', [(d, d ^ (turned if d % cores else direction) *...]
    ppermute x28, starting transfers between devices: 40.5 us -> 29.3 us  [swap(): lax.ppermute(part, 'clu', [(d, d ^ (turned if d % cores else direction) *...]
    unnamed x29 -> x20, local copies, waits for them, and re-layouts: 11.2 us -> 1.78 us
    ppermute x2, waiting for transfers between devices: 7.14 us -> 0.01 us  [apply_matrix(): outer = lax.ppermute(outer, 'clu', halo_pairs)]
    optimization_barrier x0 -> x1, local copies, waits for them, and re-layouts: none -> 4.78 us  [local(): coupling, first_coeffs = barrier((coupling, first_coeffs))]
    ppermute x4, waiting for transfers between devices: 10 us -> 13.1 us  [swap_far(): lax.ppermute(part, 'clu', [(d, (d + shift * cube) % devices) for d in ran...]
    ppermute x24, waiting for transfers between devices: 7.96 us -> 5.69 us  [swap_cores(): return lax.ppermute(part, 'clu', [(d, d ^ 1) for d in range(devices)])]
    ppermute x24, starting transfers between devices: 6.7 us -> 8.71 us  [swap_cores(): return lax.ppermute(part, 'clu', [(d, d ^ 1) for d in range(devices)])]
  transfers between devices with their start and end apart: 58 -> 58, of which waited for: 27 -> 33; matrix products, arithmetic and copies ran while one was open for 5% -> 3% of each run, Pallas kernels for 2% -> 9%
where the time goes in v8:
time: 144 us; the launch traced here: 143 us
  waiting for transfers between devices  66.5 us (46%)
  starting transfers between devices  46.5 us (32%)
  Pallas kernels  21.5 us (15%)
  local copies, waits for them, and re-layouts  6.56 us (5%)
    ppermute x28, waiting for transfers between devices, swap(): lax.ppermute(part, 'clu', [(d, d ^ (turned if d % cores else direction) *...  47.8 us
    ppermute x28, starting transfers between devices, swap(): lax.ppermute(part, 'clu', [(d, d ^ (turned if d % cores else direction) *...  29.3 us
    ppermute x4, waiting for transfers between devices, swap_far(): lax.ppermute(part, 'clu', [(d, (d + shift * cube) % devices) for d in ran...  13.1 us
    pallas_call x2, Pallas kernels, apply_matrix(): couple(source_rows, target_rows, coupling, *[got[chip] for chip in range(...  11.4 us
    ppermute x24, starting transfers between devices, swap_cores(): return lax.ppermute(part, 'clu', [(d, d ^ 1) for d in range(devices)])  8.71 us
    ppermute x4, starting transfers between devices, swap_far(): lax.ppermute(part, 'clu', [(d, (d + shift * cube) % devices) for d in ran...  5.9 us
    ppermute x24, waiting for transfers between devices, swap_cores(): return lax.ppermute(part, 'clu', [(d, d ^ 1) for d in range(devices)])  5.69 us
    pallas_call x2, Pallas kernels, apply_matrix(): finish(with_coeffs)(ranks, near_sum, edges, basis, transfer, total, *terms)  4.97 us
  transfers between devices with their start and end apart: 58, of which 33 were waited for; matrix products, arithmetic and copies ran while one was open for 3% of the time, Pallas kernels for 9%

profile of v8, /device:TPU:0, one launch (start us, length us, event | category | flops | bytes accessed | tf_op | source)
XLA Modules:
  0.0 143.2 jit_solution(660693018249578835)
XLA Ops:
  0.6 2.9 %shard_map.95 = bf16[9,32,128]{2,1,0:T(8,128)(2,1)} custom-call(s32[12]{0:T(128)} %ranks_ref.5, bf16[8,32,256]{2,1,0:T(8,128)(2,1)} %v_ref.1, bf16[8,96,256]{2,1,0:T(8,128)(2,1)} %basis_ref.3, bf16[8,96,96]{2,1,0:T(8,128)(2,1)} %transfer_ref.3), custom_call_target="tpu_custom_call" | custom-call | tf_op jit(solution)/shard_map/pallas_call | solution.py:244
  3.5 4.1 %collective-permute-start = (bf16[9,32,128]{2,1,0:T(8,128)(2,1)}, bf16[9,32,128]{2,1,0:T(8,128)(2,1)}, u32[]{:S(2)}, u32[]{:S(2)}) collective-permute-start(bf16[9,32,128]{2,1,0:T(8,128)(2,1)} %shard_map.95), channel_id=1, source_target_pairs={{0,16},{1,17},{2,18},{3,19},{4,20},{5,21},{6,22},{7,23},{8,24},{9,... | collective-permute-start | bytes 221192 | tf_op jit(solution)/shard_map/ppermute | solution.py:217
  7.6 4.8 %copy.11.in_ref = bf16[128,96,96]{2,1,0:T(8,128)(2,1)} copy(bf16[128,96,96]{0,2,1:T(8,128)(2,1)} %param.12) | data formatting | bytes 4718592 | tf_op jit(solution)/shard_map/optimization_barrier | solution.py:363
  12.5 0.8 copy-done.7
  13.3 1.1 pad_maximum_fusion.refs_0_
  14.4 1.6 %collective-permute-start.3 = (bf16[2,9,32,128]{3,2,1,0:T(8,128)(2,1)S(1)}, bf16[2,9,32,128]{3,2,1,0:T(8,128)(2,1)}, u32[]{:S(2)}, u32[]{:S(2)}) collective-permute-start(bf16[2,9,32,128]{3,2,1,0:T(8,128)(2,1)S(1)} %pad_maximum_fusion.refs_0_), channel_id=1, source_target_pairs={{0,8},{1,3},{2,10},{3,1},{4,12},{5,7},{6,14},{7,5},{8,0},{9,11},{1... | collective-permute-start | bytes 442376 | tf_op jit(solution)/shard_map/ppermute | solution.py:221
  16.0 1.5 %collective-permute-start.2 = (bf16[2,9,32,128]{3,2,1,0:T(8,128)(2,1)S(1)}, bf16[2,9,32,128]{3,2,1,0:T(8,128)(2,1)}, u32[]{:S(2)}, u32[]{:S(2)}) collective-permute-start(bf16[2,9,32,128]{3,2,1,0:T(8,128)(2,1)S(1)} %pad_maximum_fusion.refs_0_), channel_id=1, source_target_pairs={{0,4},{1,9},{2,6},{3,11},{4,0},{5,13},{6,2},{7,15},{8,12},{9,1},{1... | collective-permute-start | bytes 442376 | tf_op jit(solution)/shard_map/ppermute | solution.py:221
  17.5 1.5 %collective-permute-start.1 = (bf16[2,9,32,128]{3,2,1,0:T(8,128)(2,1)S(1)}, bf16[2,9,32,128]{3,2,1,0:T(8,128)(2,1)}, u32[]{:S(2)}, u32[]{:S(2)}) collective-permute-start(bf16[2,9,32,128]{3,2,1,0:T(8,128)(2,1)S(1)} %pad_maximum_fusion.refs_0_), channel_id=1, source_target_pairs={{0,2},{1,5},{2,0},{3,7},{4,6},{5,1},{6,4},{7,3},{8,10},{9,13},{10,... | collective-permute-start | bytes 442376 | tf_op jit(solution)/shard_map/ppermute | solution.py:221
  19.0 2.0 %collective-permute-done.3.refs_4_ = bf16[2,9,32,128]{3,2,1,0:T(8,128)(2,1)} collective-permute-done((bf16[2,9,32,128]{3,2,1,0:T(8,128)(2,1)S(1)}, bf16[2,9,32,128]{3,2,1,0:T(8,128)(2,1)}, u32[]{:S(2)}, u32[]{:S(2)}) %collective-permute-start.3) | collective-permute-done | bytes 147488 | tf_op jit(solution)/shard_map/ppermute | solution.py:221
  21.1 1.3 collective-permute-done.2.refs_2_
  22.8 1.1 collective-permute-start.4
  24.3 0.9 collective-permute-start.5
  25.2 0.6 shard_map.97.near_ref
  25.8 2.5 %collective-permute-done.4.refs_3_ = bf16[2,9,32,128]{3,2,1,0:T(8,128)(2,1)} collective-permute-done((bf16[2,9,32,128]{3,2,1,0:T(8,128)(2,1)}, bf16[2,9,32,128]{3,2,1,0:T(8,128)(2,1)}, u32[]{:S(2)}, u32[]{:S(2)}) %collective-permute-start.4) | collective-permute-done | bytes 147488 | tf_op jit(solution)/shard_map/ppermute | solution.py:221
  28.3 1.0 collective-permute-done.6.refs_6_
  30.8 1.6 %collective-permute-start.8 = (bf16[2,9,32,128]{3,2,1,0:T(8,128)(2,1)}, bf16[2,9,32,128]{3,2,1,0:T(8,128)(2,1)S(1)}, u32[]{:S(2)}, u32[]{:S(2)}) collective-permute-start(bf16[2,9,32,128]{3,2,1,0:T(8,128)(2,1)} %collective-permute-done.4.refs_3_), channel_id=1, source_target_pairs={{0,8},{1,3},{2,10},{3,1},{4,12},{5,7},{6,14},{7,5},{8,0},{9,11},{1... | collective-permute-start | bytes 442376 | tf_op jit(solution)/shard_map/ppermute | solution.py:221
  32.4 3.8 %collective-permute-done.8.refs_7_ = bf16[2,9,32,128]{3,2,1,0:T(8,128)(2,1)S(1)} collective-permute-done((bf16[2,9,32,128]{3,2,1,0:T(8,128)(2,1)}, bf16[2,9,32,128]{3,2,1,0:T(8,128)(2,1)S(1)}, u32[]{:S(2)}, u32[]{:S(2)}) %collective-permute-start.8) | collective-permute-done | bytes 147488 | tf_op jit(solution)/shard_map/ppermute | solution.py:221
  36.8 1.3 collective-permute-start.17
  38.1 1.7 %collective-permute-start.16 = (bf16[2,9,32,128]{3,2,1,0:T(8,128)(2,1)S(1)}, bf16[2,9,32,128]{3,2,1,0:T(8,128)(2,1)S(1)}, u32[]{:S(2)}, u32[]{:S(2)}) collective-permute-start(bf16[2,9,32,128]{3,2,1,0:T(8,128)(2,1)S(1)} %collective-permute-done.8.refs_7_), channel_id=1, source_target_pairs={{0,1},{1,0},{2,3},{3,2},{4,5},{5,4},{6,7},{7,6},{8,9},{9,8},{10,11... | collective-permute-start | bytes 442376 | tf_op jit(solution)/shard_map/ppermute | solution.py:226
  39.9 0.9 collective-permute-done.16.refs_15_
  40.8 6.0 %shard_map.98 = (bf16[4,2,9,32,128]{4,3,2,1,0:T(8,128)(2,1)S(1)}, bf16[4,2,9,32,128]{4,3,2,1,0:T(8,128)(2,1)S(1)}, bf16[4,2,9,32,128]{4,3,2,1,0:T(8,128)(2,1)S(1)}, bf16[4,2,9,32,128]{4,3,2,1,0:T(8,128)(2,1)S(1)}) custom-call(s32[128]{0:T(128)S(1)} %get-tuple-element.158.source_ref, s32[128]{0:T(128)S(1)} %get-tuple-element.159.target_ref, ...), custom_call_target="tpu_custom_call" | custom-call | flops 75497472 | bytes 10485760 | tf_op jit(solution)/shard_map/pallas_call | solution.py:342
  47.4 1.5 %collective-permute-done.20.swap_ref = bf16[4,2,9,32,128]{4,3,2,1,0:T(8,128)(2,1)S(1)} collective-permute-done((bf16[4,2,9,32,128]{4,3,2,1,0:T(8,128)(2,1)S(1)}, bf16[4,2,9,32,128]{4,3,2,1,0:T(8,128)(2,1)S(1)}, u32[]{:S(2)}, u32[]{:S(2)}) %collective-permute-start.20) | collective-permute-done | bytes 589856 | tf_op jit(solution)/shard_map/ppermute | solution.py:226
  49.1 2.7 %collective-permute-start.21 = (bf16[2,9,32,128]{3,2,1,0:T(8,128)(2,1)S(1)}, bf16[2,9,32,128]{3,2,1,0:T(8,128)(2,1)S(1)}, u32[]{:S(2)}, u32[]{:S(2)}) collective-permute-start(bf16[2,9,32,128]{3,2,1,0:T(8,128)(2,1)S(1)} %get-tuple-element.104), channel_id=1, source_target_pairs={{0,8},{1,3},{2,10},{3,1},{4,12},{5,7},{6,14},{7,5},{8,0},{9,11},{1... | collective-permute-start | bytes 442376 | tf_op jit(solution)/shard_map/ppermute | solution.py:221
  51.8 0.6 collective-permute-start.22
  53.0 3.5 %collective-permute-done.21 = bf16[2,9,32,128]{3,2,1,0:T(8,128)(2,1)S(1)} collective-permute-done((bf16[2,9,32,128]{3,2,1,0:T(8,128)(2,1)S(1)}, bf16[2,9,32,128]{3,2,1,0:T(8,128)(2,1)S(1)}, u32[]{:S(2)}, u32[]{:S(2)}) %collective-permute-start.21) | collective-permute-done | bytes 147488 | tf_op jit(solution)/shard_map/ppermute | solution.py:221
  56.5 1.3 collective-permute-done.22.yz_ref
  57.8 1.2 collective-permute-start.24
  59.2 0.9 collective-permute-start.26
  60.1 0.8 collective-permute-start.27
  60.9 2.1 %collective-permute-done.24.x_ref = bf16[2,9,32,128]{3,2,1,0:T(8,128)(2,1)S(1)} collective-permute-done((bf16[2,9,32,128]{3,2,1,0:T(8,128)(2,1)S(1)}, bf16[2,9,32,128]{3,2,1,0:T(8,128)(2,1)S(1)}, u32[]{:S(2)}, u32[]{:S(2)}) %collective-permute-start.24) | collective-permute-done | bytes 147488 | tf_op jit(solution)/shard_map/ppermute | solution.py:221
  63.1 1.0 collective-permute-start.25
  64.1 0.7 collective-permute-done.26.y_ref
  65.3 3.0 %collective-permute-done.25.x_ref = bf16[2,9,32,128]{3,2,1,0:T(8,128)(2,1)S(1)} collective-permute-done((bf16[2,9,32,128]{3,2,1,0:T(8,128)(2,1)S(1)}, bf16[2,9,32,128]{3,2,1,0:T(8,128)(2,1)S(1)}, u32[]{:S(2)}, u32[]{:S(2)}) %collective-permute-start.25) | collective-permute-done | bytes 147488 | tf_op jit(solution)/shard_map/ppermute | solution.py:221
  68.4 1.1 collective-permute-start.28
  70.0 0.7 collective-permute-done.7.inner_ref
  71.0 3.5 %collective-permute-done.28.rest_0_ = bf16[9,32,128]{2,1,0:T(8,128)(2,1)S(1)} collective-permute-done((bf16[9,32,128]{2,1,0:T(8,128)(2,1)S(1)}, bf16[9,32,128]{2,1,0:T(8,128)(2,1)S(1)}, u32[]{:S(2)}, u32[]{:S(2)}) %collective-permute-start.28) | collective-permute-done | bytes 73760 | tf_op jit(solution)/shard_map/ppermute | solution.py:217
  74.5 2.5 %shard_map.104 = (bf16[8,32,256]{2,1,0:T(8,128)(2,1)}, bf16[9,32,128]{2,1,0:T(8,128)(2,1)S(1)}) custom-call(s32[12]{0:T(128)S(1)} %copy-done.6, f32[8,32,256]{2,1,0:T(8,128)S(1)} %shard_map.97.near_ref, f32[2,32,256]{2,1,0:T(8,128)S(1)} %shard_map.99.edge_ref, bf16[8,96,256]{2,1,0:T(8,128)(2,1)S(1)} %copy-done.2, bf16[8,96,96]{2,1,0:T(8,128)(2,1)S(1)} %copy-done.3, ...), custom_call_target="tpu_custom_call" | custom-call | tf_op jit(solution)/shard_map/pallas_call | solution.py:361
  77.3 5.3 %collective-permute-done.29 = bf16[9,32,128]{2,1,0:T(8,128)(2,1)S(1)} collective-permute-done((bf16[9,32,128]{2,1,0:T(8,128)(2,1)S(1)}, bf16[9,32,128]{2,1,0:T(8,128)(2,1)S(1)}, u32[]{:S(2)}, u32[]{:S(2)}) %collective-permute-start.29) | collective-permute-done | bytes 73760 | tf_op jit(solution)/shard_map/ppermute | solution.py:217
  82.8 0.7 collective-permute-start.31
  83.4 1.4 collective-permute-start.30
  84.9 3.8 %collective-permute-done.32.refs_4_ = bf16[2,9,32,128]{3,2,1,0:T(8,128)(2,1)S(1)} collective-permute-done((bf16[2,9,32,128]{3,2,1,0:T(8,128)(2,1)S(1)}, bf16[2,9,32,128]{3,2,1,0:T(8,128)(2,1)S(1)}, u32[]{:S(2)}, u32[]{:S(2)}) %collective-permute-start.32) | collective-permute-done | bytes 147488 | tf_op jit(solution)/shard_map/ppermute | solution.py:221
  88.7 1.3 collective-permute-done.30.refs_1_
  90.0 1.4 collective-permute-start.33
  91.4 2.1 %collective-permute-start.35 = (bf16[2,9,32,128]{3,2,1,0:T(8,128)(2,1)S(1)}, bf16[2,9,32,128]{3,2,1,0:T(8,128)(2,1)S(1)}, u32[]{:S(2)}, u32[]{:S(2)}) collective-permute-start(bf16[2,9,32,128]{3,2,1,0:T(8,128)(2,1)S(1)} %collective-permute-done.31.refs_2_), channel_id=1, source_target_pairs={{0,8},{1,3},{2,10},{3,1},{4,12},{5,7},{6,14},{7,5},{8,0},{9,11},{1... | collective-permute-start | bytes 442376 | tf_op jit(solution)/shard_map/ppermute | solution.py:221
  93.5 1.2 collective-permute-start.34
  94.7 0.9 copy-done.5
  96.6 2.0 %collective-permute-done.34.refs_5_ = bf16[2,9,32,128]{3,2,1,0:T(8,128)(2,1)S(1)} collective-permute-done((bf16[2,9,32,128]{3,2,1,0:T(8,128)(2,1)S(1)}, bf16[2,9,32,128]{3,2,1,0:T(8,128)(2,1)S(1)}, u32[]{:S(2)}, u32[]{:S(2)}) %collective-permute-start.34) | collective-permute-done | bytes 147488 | tf_op jit(solution)/shard_map/ppermute | solution.py:221
  99.7 5.1 %collective-permute-done.37.refs_7_ = bf16[2,9,32,128]{3,2,1,0:T(8,128)(2,1)S(1)} collective-permute-done((bf16[2,9,32,128]{3,2,1,0:T(8,128)(2,1)S(1)}, bf16[2,9,32,128]{3,2,1,0:T(8,128)(2,1)S(1)}, u32[]{:S(2)}, u32[]{:S(2)}) %collective-permute-start.37) | collective-permute-done | bytes 147488 | tf_op jit(solution)/shard_map/ppermute | solution.py:221
  105.8 1.3 collective-permute-start.46
  107.2 5.4 %shard_map.106 = (bf16[4,2,9,32,128]{4,3,2,1,0:T(8,128)(2,1)S(1)}, bf16[4,2,9,32,128]{4,3,2,1,0:T(8,128)(2,1)S(1)}, bf16[4,2,9,32,128]{4,3,2,1,0:T(8,128)(2,1)S(1)}, bf16[4,2,9,32,128]{4,3,2,1,0:T(8,128)(2,1)S(1)}) custom-call(s32[128]{0:T(128)S(1)} %get-tuple-element.158.source_ref, s32[128]{0:T(128)S(1)} %get-tuple-element.159.target_ref, ...), custom_call_target="tpu_custom_call" | custom-call | flops 75497472 | bytes 10485760 | tf_op jit(solution)/shard_map/pallas_call | solution.py:342
  112.5 1.7 %collective-permute-start.49 = (bf16[4,2,9,32,128]{4,3,2,1,0:T(8,128)(2,1)S(1)}, bf16[4,2,9,32,128]{4,3,2,1,0:T(8,128)(2,1)S(1)}, u32[]{:S(2)}, u32[]{:S(2)}) collective-permute-start(bf16[4,2,9,32,128]{4,3,2,1,0:T(8,128)(2,1)S(1)} %get-tuple-element.141), channel_id=1, source_target_pairs={{0,1},{1,0},{2,3},{3,2},{4,5},{5,4},{6,7},{7,6},{8,9},{9,8},{10,11... | collective-permute-start | bytes 1769480 | tf_op jit(solution)/shard_map/ppermute | solution.py:226
  114.3 1.6 %collective-permute-done.49.swap_ref = bf16[4,2,9,32,128]{4,3,2,1,0:T(8,128)(2,1)S(1)} collective-permute-done((bf16[4,2,9,32,128]{4,3,2,1,0:T(8,128)(2,1)S(1)}, bf16[4,2,9,32,128]{4,3,2,1,0:T(8,128)(2,1)S(1)}, u32[]{:S(2)}, u32[]{:S(2)}) %collective-permute-start.49) | collective-permute-done | bytes 589856 | tf_op jit(solution)/shard_map/ppermute | solution.py:226
  116.0 2.4 %collective-permute-start.50 = (bf16[2,9,32,128]{3,2,1,0:T(8,128)(2,1)S(1)}, bf16[2,9,32,128]{3,2,1,0:T(8,128)(2,1)S(1)}, u32[]{:S(2)}, u32[]{:S(2)}) collective-permute-start(bf16[2,9,32,128]{3,2,1,0:T(8,128)(2,1)S(1)} %get-tuple-element.142), channel_id=1, source_target_pairs={{0,8},{1,3},{2,10},{3,1},{4,12},{5,7},{6,14},{7,5},{8,0},{9,11},{1... | collective-permute-start | bytes 442376 | tf_op jit(solution)/shard_map/ppermute | solution.py:221
  118.4 4.7 %collective-permute-done.50 = bf16[2,9,32,128]{3,2,1,0:T(8,128)(2,1)S(1)} collective-permute-done((bf16[2,9,32,128]{3,2,1,0:T(8,128)(2,1)S(1)}, bf16[2,9,32,128]{3,2,1,0:T(8,128)(2,1)S(1)}, u32[]{:S(2)}, u32[]{:S(2)}) %collective-permute-start.50) | collective-permute-done | bytes 147488 | tf_op jit(solution)/shard_map/ppermute | solution.py:221
  123.1 1.0 collective-permute-done.51.yz_ref
  124.1 1.5 %collective-permute-start.53 = (bf16[2,9,32,128]{3,2,1,0:T(8,128)(2,1)S(1)}, bf16[2,9,32,128]{3,2,1,0:T(8,128)(2,1)S(1)}, u32[]{:S(2)}, u32[]{:S(2)}) collective-permute-start(bf16[2,9,32,128]{3,2,1,0:T(8,128)(2,1)S(1)} %add_convert_fusion), channel_id=1, source_target_pairs={{0,4},{1,9},{2,6},{3,11},{4,0},{5,13},{6,2},{7,15},{8,12},{9,1},{1... | collective-permute-start | bytes 442376 | tf_op jit(solution)/shard_map/ppermute | solution.py:221
  125.8 0.6 collective-permute-start.55
  126.4 1.2 collective-permute-start.56
  127.6 1.7 %collective-permute-done.53.x_ref = bf16[2,9,32,128]{3,2,1,0:T(8,128)(2,1)S(1)} collective-permute-done((bf16[2,9,32,128]{3,2,1,0:T(8,128)(2,1)S(1)}, bf16[2,9,32,128]{3,2,1,0:T(8,128)(2,1)S(1)}, u32[]{:S(2)}, u32[]{:S(2)}) %collective-permute-start.53) | collective-permute-done | bytes 147488 | tf_op jit(solution)/shard_map/ppermute | solution.py:221
  129.5 2.6 %collective-permute-done.55.y_ref = bf16[2,9,32,128]{3,2,1,0:T(8,128)(2,1)S(1)} collective-permute-done((bf16[2,9,32,128]{3,2,1,0:T(8,128)(2,1)S(1)}, bf16[2,9,32,128]{3,2,1,0:T(8,128)(2,1)S(1)}, u32[]{:S(2)}, u32[]{:S(2)}) %collective-permute-start.55) | collective-permute-done | bytes 147488 | tf_op jit(solution)/shard_map/ppermute | solution.py:221
  132.1 2.5 %collective-permute-done.54.x_ref = bf16[2,9,32,128]{3,2,1,0:T(8,128)(2,1)S(1)} collective-permute-done((bf16[2,9,32,128]{3,2,1,0:T(8,128)(2,1)S(1)}, bf16[2,9,32,128]{3,2,1,0:T(8,128)(2,1)S(1)}, u32[]{:S(2)}, u32[]{:S(2)}) %collective-permute-start.54) | collective-permute-done | bytes 147488 | tf_op jit(solution)/shard_map/ppermute | solution.py:221
  135.5 0.7 collective-permute-done.36.inner_ref
  136.5 4.3 %collective-permute-done.57.rest_0_ = bf16[9,32,128]{2,1,0:T(8,128)(2,1)S(1)} collective-permute-done((bf16[9,32,128]{2,1,0:T(8,128)(2,1)S(1)}, bf16[9,32,128]{2,1,0:T(8,128)(2,1)S(1)}, u32[]{:S(2)}, u32[]{:S(2)}) %collective-permute-start.57) | collective-permute-done | bytes 73760 | tf_op jit(solution)/shard_map/ppermute | solution.py:217
  140.8 2.5 %shard_map.112 = bf16[8,32,256]{2,1,0:T(8,128)(2,1)} custom-call(s32[12]{0:T(128)S(1)} %copy-done.6, f32[8,32,256]{2,1,0:T(8,128)S(1)} %shard_map.105.near_ref, f32[2,32,256]{2,1,0:T(8,128)S(1)} %shard_map.107.edge_ref, bf16[8,96,256]{2,1,0:T(8,128)(2,1)S(1)} %copy-done.2, bf16[8,96,96]{2,1,0:T(8,128)(2,1)S(1)} %copy-done.3, ...), custom_call_target="tpu_custom_call" | custom-call | tf_op jit(solution)/shard_map/pallas_call | solution.py:361
  (98 shorter events, 11.2 us)
Async XLA Ops:
  3.5 8.9 %collective-permute-start = (bf16[9,32,128]{2,1,0:T(8,128)(2,1)}, bf16[9,32,128]{2,1,0:T(8,128)(2,1)}, u32[]{:S(2)}, u32[]{:S(2)}) collective-permute-start(bf16[9,32,128]{2,1,0:T(8,128)(2,1)} %shard_map.95), channel_id=1, source_target_pairs={{0,16},{1,17},{2,18},{3,19},{4,20},{5,21},{6,22},{7,23},{8,24},{9,... | collective-permute-start | bytes 221192 | tf_op jit(solution)/shard_map/ppermute | solution.py:217
  12.4 12.8 %copy-start = (bf16[8,3,256,256]{3,2,1,0:T(8,128)(2,1)S(1)}, bf16[8,3,256,256]{3,2,1,0:T(8,128)(2,1)}, u32[]{:S(2)}) copy-start(bf16[8,3,256,256]{3,2,1,0:T(8,128)(2,1)} %last_ref.3) | copy-start | bytes 9437188
  12.4 12.8 %copy-start.4 = (bf16[8,32,256]{2,1,0:T(8,128)(2,1)S(1)}, bf16[8,32,256]{2,1,0:T(8,128)(2,1)}, u32[]{:S(2)}) copy-start(bf16[8,32,256]{2,1,0:T(8,128)(2,1)} %v_ref.1) | copy-start | bytes 393220
  12.4 27.4 %copy-start.8 = (s32[128]{0:T(128)S(1)}, s32[128]{0:T(128)}, u32[]{:S(2)}) copy-start(s32[128]{0:T(128)} %param.14) | copy-start | bytes 1540
  12.4 27.4 %copy-start.9 = (s32[128]{0:T(128)S(1)}, s32[128]{0:T(128)}, u32[]{:S(2)}) copy-start(s32[128]{0:T(128)} %param.15) | copy-start | bytes 1540
  14.4 6.7 %collective-permute-start.3 = (bf16[2,9,32,128]{3,2,1,0:T(8,128)(2,1)S(1)}, bf16[2,9,32,128]{3,2,1,0:T(8,128)(2,1)}, u32[]{:S(2)}, u32[]{:S(2)}) collective-permute-start(bf16[2,9,32,128]{3,2,1,0:T(8,128)(2,1)S(1)} %pad_maximum_fusion.refs_0_), channel_id=1, source_target_pairs={{0,8},{1,3},{2,10},{3,1},{4,12},{5,7},{6,14},{7,5},{8,0},{9,11},{1... | collective-permute-start | bytes 442376 | tf_op jit(solution)/shard_map/ppermute | solution.py:221
  16.0 6.3 %collective-permute-start.2 = (bf16[2,9,32,128]{3,2,1,0:T(8,128)(2,1)S(1)}, bf16[2,9,32,128]{3,2,1,0:T(8,128)(2,1)}, u32[]{:S(2)}, u32[]{:S(2)}) collective-permute-start(bf16[2,9,32,128]{3,2,1,0:T(8,128)(2,1)S(1)} %pad_maximum_fusion.refs_0_), channel_id=1, source_target_pairs={{0,4},{1,9},{2,6},{3,11},{4,0},{5,13},{6,2},{7,15},{8,12},{9,1},{1... | collective-permute-start | bytes 442376 | tf_op jit(solution)/shard_map/ppermute | solution.py:221
  17.5 5.2 %collective-permute-start.1 = (bf16[2,9,32,128]{3,2,1,0:T(8,128)(2,1)S(1)}, bf16[2,9,32,128]{3,2,1,0:T(8,128)(2,1)}, u32[]{:S(2)}, u32[]{:S(2)}) collective-permute-start(bf16[2,9,32,128]{3,2,1,0:T(8,128)(2,1)S(1)} %pad_maximum_fusion.refs_0_), channel_id=1, source_target_pairs={{0,2},{1,5},{2,0},{3,7},{4,6},{5,1},{6,4},{7,3},{8,10},{9,13},{10,... | collective-permute-start | bytes 442376 | tf_op jit(solution)/shard_map/ppermute | solution.py:221
  22.8 5.6 %collective-permute-start.4 = (bf16[2,9,32,128]{3,2,1,0:T(8,128)(2,1)}, bf16[2,9,32,128]{3,2,1,0:T(8,128)(2,1)}, u32[]{:S(2)}, u32[]{:S(2)}) collective-permute-start(bf16[2,9,32,128]{3,2,1,0:T(8,128)(2,1)} %collective-permute-done.1.refs_1_), channel_id=1, source_target_pairs={{0,4},{1,9},{2,6},{3,11},{4,0},{5,13},{6,2},{7,15},{8,12},{9,1},{1... | collective-permute-start | bytes 442376 | tf_op jit(solution)/shard_map/ppermute | solution.py:221
  23.9 5.5 %collective-permute-start.6 = (bf16[2,9,32,128]{3,2,1,0:T(8,128)(2,1)}, bf16[2,9,32,128]{3,2,1,0:T(8,128)(2,1)}, u32[]{:S(2)}, u32[]{:S(2)}) collective-permute-start(bf16[2,9,32,128]{3,2,1,0:T(8,128)(2,1)} %collective-permute-done.2.refs_2_), channel_id=1, source_target_pairs={{0,8},{1,3},{2,10},{3,1},{4,12},{5,7},{6,14},{7,5},{8,0},{9,11},{1... | collective-permute-start | bytes 442376 | tf_op jit(solution)/shard_map/ppermute | solution.py:221
  24.3 5.5 %collective-permute-start.5 = (bf16[2,9,32,128]{3,2,1,0:T(8,128)(2,1)}, bf16[2,9,32,128]{3,2,1,0:T(8,128)(2,1)}, u32[]{:S(2)}, u32[]{:S(2)}) collective-permute-start(bf16[2,9,32,128]{3,2,1,0:T(8,128)(2,1)} %collective-permute-done.3.refs_4_), channel_id=1, source_target_pairs={{0,2},{1,5},{2,0},{3,7},{4,6},{5,1},{6,4},{7,3},{8,10},{9,13},{10,... | collective-permute-start | bytes 442376 | tf_op jit(solution)/shard_map/ppermute | solution.py:221
  25.2 15.6 %copy-start.1 = (bf16[128,96,96]{2,1,0:T(8,128)(2,1)S(1)}, bf16[128,96,96]{2,1,0:T(8,128)(2,1)}, u32[]{:S(2)}) copy-start(bf16[128,96,96]{2,1,0:T(8,128)(2,1)} %shard_map.96.coupling_ref) | copy-start | bytes 7077892
  29.8 6.4 %collective-permute-start.9 = (bf16[2,9,32,128]{3,2,1,0:T(8,128)(2,1)S(1)}, bf16[2,9,32,128]{3,2,1,0:T(8,128)(2,1)S(1)}, u32[]{:S(2)}, u32[]{:S(2)}) collective-permute-start(bf16[2,9,32,128]{3,2,1,0:T(8,128)(2,1)S(1)} %pad_maximum_fusion.refs_0_), channel_id=1, source_target_pairs={{0,1},{1,0},{2,3},{3,2},{4,5},{5,4},{6,7},{7,6},{8,9},{9,8},{10,11... | collective-permute-start | bytes 442376 | tf_op jit(solution)/shard_map/ppermute | solution.py:226
  29.8 6.9 %collective-permute-start.10 = (bf16[2,9,32,128]{3,2,1,0:T(8,128)(2,1)}, bf16[2,9,32,128]{3,2,1,0:T(8,128)(2,1)S(1)}, u32[]{:S(2)}, u32[]{:S(2)}) collective-permute-start(bf16[2,9,32,128]{3,2,1,0:T(8,128)(2,1)} %collective-permute-done.1.refs_1_), channel_id=1, source_target_pairs={{0,1},{1,0},{2,3},{3,2},{4,5},{5,4},{6,7},{7,6},{8,9},{9,8},{10,11... | collective-permute-start | bytes 442376 | tf_op jit(solution)/shard_map/ppermute | solution.py:226
  30.3 6.5 %collective-permute-start.11 = (bf16[2,9,32,128]{3,2,1,0:T(8,128)(2,1)}, bf16[2,9,32,128]{3,2,1,0:T(8,128)(2,1)S(1)}, u32[]{:S(2)}, u32[]{:S(2)}) collective-permute-start(bf16[2,9,32,128]{3,2,1,0:T(8,128)(2,1)} %collective-permute-done.2.refs_2_), channel_id=1, source_target_pairs={{0,1},{1,0},{2,3},{3,2},{4,5},{5,4},{6,7},{7,6},{8,9},{9,8},{10,11... | collective-permute-start | bytes 442376 | tf_op jit(solution)/shard_map/ppermute | solution.py:226
  30.3 7.7 %collective-permute-start.13 = (bf16[2,9,32,128]{3,2,1,0:T(8,128)(2,1)}, bf16[2,9,32,128]{3,2,1,0:T(8,128)(2,1)S(1)}, u32[]{:S(2)}, u32[]{:S(2)}) collective-permute-start(bf16[2,9,32,128]{3,2,1,0:T(8,128)(2,1)} %collective-permute-done.3.refs_4_), channel_id=1, source_target_pairs={{0,1},{1,0},{2,3},{3,2},{4,5},{5,4},{6,7},{7,6},{8,9},{9,8},{10,11... | collective-permute-start | bytes 442376 | tf_op jit(solution)/shard_map/ppermute | solution.py:226
  30.8 5.4 %collective-permute-start.8 = (bf16[2,9,32,128]{3,2,1,0:T(8,128)(2,1)}, bf16[2,9,32,128]{3,2,1,0:T(8,128)(2,1)S(1)}, u32[]{:S(2)}, u32[]{:S(2)}) collective-permute-start(bf16[2,9,32,128]{3,2,1,0:T(8,128)(2,1)} %collective-permute-done.4.refs_3_), channel_id=1, source_target_pairs={{0,8},{1,3},{2,10},{3,1},{4,12},{5,7},{6,14},{7,5},{8,0},{9,11},{1... | collective-permute-start | bytes 442376 | tf_op jit(solution)/shard_map/ppermute | solution.py:221
  36.2 3.7 %collective-permute-start.12 = (bf16[2,9,32,128]{3,2,1,0:T(8,128)(2,1)}, bf16[2,9,32,128]{3,2,1,0:T(8,128)(2,1)S(1)}, u32[]{:S(2)}, u32[]{:S(2)}) collective-permute-start(bf16[2,9,32,128]{3,2,1,0:T(8,128)(2,1)} %collective-permute-done.4.refs_3_), channel_id=1, source_target_pairs={{0,1},{1,0},{2,3},{3,2},{4,5},{5,4},{6,7},{7,6},{8,9},{9,8},{10,11... | collective-permute-start | bytes 442376 | tf_op jit(solution)/shard_map/ppermute | solution.py:226
  36.2 3.7 %collective-permute-start.14 = (bf16[2,9,32,128]{3,2,1,0:T(8,128)(2,1)}, bf16[2,9,32,128]{3,2,1,0:T(8,128)(2,1)S(1)}, u32[]{:S(2)}, u32[]{:S(2)}) collective-permute-start(bf16[2,9,32,128]{3,2,1,0:T(8,128)(2,1)} %collective-permute-done.5.refs_5_), channel_id=1, source_target_pairs={{0,1},{1,0},{2,3},{3,2},{4,5},{5,4},{6,7},{7,6},{8,9},{9,8},{10,11... | collective-permute-start | bytes 442376 | tf_op jit(solution)/shard_map/ppermute | solution.py:226
  36.7 3.2 %collective-permute-start.15 = (bf16[2,9,32,128]{3,2,1,0:T(8,128)(2,1)}, bf16[2,9,32,128]{3,2,1,0:T(8,128)(2,1)S(1)}, u32[]{:S(2)}, u32[]{:S(2)}) collective-permute-start(bf16[2,9,32,128]{3,2,1,0:T(8,128)(2,1)} %collective-permute-done.6.refs_6_), channel_id=1, source_target_pairs={{0,1},{1,0},{2,3},{3,2},{4,5},{5,4},{6,7},{7,6},{8,9},{9,8},{10,11... | collective-permute-start | bytes 442376 | tf_op jit(solution)/shard_map/ppermute | solution.py:226
  36.8 10.1 %collective-permute-start.17 = (bf16[1,32,256]{2,1,0:T(8,128)(2,1)S(1)}, bf16[1,32,256]{2,1,0:T(8,128)(2,1)S(1)}, u32[]{:S(2)}, u32[]{:S(2)}) collective-permute-start(bf16[1,32,256]{2,1,0:T(8,128)(2,1)S(1)} %get-tuple-element.98), channel_id=1, source_target_pairs={{1,3},{3,5},{5,7},{7,9},{9,11},{11,13},{13,15},{15,17},{17,19},{19... | collective-permute-start | bytes 49160 | tf_op jit(solution)/shard_map/ppermute | solution.py:341
  38.1 2.7 %collective-permute-start.16 = (bf16[2,9,32,128]{3,2,1,0:T(8,128)(2,1)S(1)}, bf16[2,9,32,128]{3,2,1,0:T(8,128)(2,1)S(1)}, u32[]{:S(2)}, u32[]{:S(2)}) collective-permute-start(bf16[2,9,32,128]{3,2,1,0:T(8,128)(2,1)S(1)} %collective-permute-done.8.refs_7_), channel_id=1, source_target_pairs={{0,1},{1,0},{2,3},{3,2},{4,5},{5,4},{6,7},{7,6},{8,9},{9,8},{10,11... | collective-permute-start | bytes 442376 | tf_op jit(solution)/shard_map/ppermute | solution.py:226
  46.9 2.1 %collective-permute-start.20 = (bf16[4,2,9,32,128]{4,3,2,1,0:T(8,128)(2,1)S(1)}, bf16[4,2,9,32,128]{4,3,2,1,0:T(8,128)(2,1)S(1)}, u32[]{:S(2)}, u32[]{:S(2)}) collective-permute-start(bf16[4,2,9,32,128]{4,3,2,1,0:T(8,128)(2,1)S(1)} %get-tuple-element.103), channel_id=1, source_target_pairs={{0,1},{1,0},{2,3},{3,2},{4,5},{5,4},{6,7},{7,6},{8,9},{9,8},{10,11... | collective-permute-start | bytes 1769480 | tf_op jit(solution)/shard_map/ppermute | solution.py:226
  47.3 11.8 %collective-permute-start.19 = (bf16[4,2,9,32,128]{4,3,2,1,0:T(8,128)(2,1)S(1)}, bf16[4,2,9,32,128]{4,3,2,1,0:T(8,128)(2,1)S(1)}, u32[]{:S(2)}, u32[]{:S(2)}) collective-permute-start(bf16[4,2,9,32,128]{4,3,2,1,0:T(8,128)(2,1)S(1)} %get-tuple-element.101), channel_id=1, source_target_pairs={{0,1},{1,0},{2,3},{3,2},{4,5},{5,4},{6,7},{7,6},{8,9},{9,8},{10,11... | collective-permute-start | bytes 1769480 | tf_op jit(solution)/shard_map/ppermute | solution.py:226
  49.1 7.4 %collective-permute-start.21 = (bf16[2,9,32,128]{3,2,1,0:T(8,128)(2,1)S(1)}, bf16[2,9,32,128]{3,2,1,0:T(8,128)(2,1)S(1)}, u32[]{:S(2)}, u32[]{:S(2)}) collective-permute-start(bf16[2,9,32,128]{3,2,1,0:T(8,128)(2,1)S(1)} %get-tuple-element.104), channel_id=1, source_target_pairs={{0,8},{1,3},{2,10},{3,1},{4,12},{5,7},{6,14},{7,5},{8,0},{9,11},{1... | collective-permute-start | bytes 442376 | tf_op jit(solution)/shard_map/ppermute | solution.py:221
  51.8 6.0 %collective-permute-start.22 = (bf16[2,9,32,128]{3,2,1,0:T(8,128)(2,1)S(1)}, bf16[2,9,32,128]{3,2,1,0:T(8,128)(2,1)S(1)}, u32[]{:S(2)}, u32[]{:S(2)}) collective-permute-start(bf16[2,9,32,128]{3,2,1,0:T(8,128)(2,1)S(1)} %get-tuple-element.105), channel_id=1, source_target_pairs={{0,4},{1,9},{2,6},{3,11},{4,0},{5,13},{6,2},{7,15},{8,12},{9,1},{1... | collective-permute-start | bytes 442376 | tf_op jit(solution)/shard_map/ppermute | solution.py:221
  52.4 5.4 %collective-permute-start.23 = (bf16[2,9,32,128]{3,2,1,0:T(8,128)(2,1)S(1)}, bf16[2,9,32,128]{3,2,1,0:T(8,128)(2,1)S(1)}, u32[]{:S(2)}, u32[]{:S(2)}) collective-permute-start(bf16[2,9,32,128]{3,2,1,0:T(8,128)(2,1)S(1)} %get-tuple-element.106), channel_id=1, source_target_pairs={{0,2},{1,5},{2,0},{3,7},{4,6},{5,1},{6,4},{7,3},{8,10},{9,13},{10,... | collective-permute-start | bytes 442376 | tf_op jit(solution)/shard_map/ppermute | solution.py:221
  57.8 5.2 %collective-permute-start.24 = (bf16[2,9,32,128]{3,2,1,0:T(8,128)(2,1)S(1)}, bf16[2,9,32,128]{3,2,1,0:T(8,128)(2,1)S(1)}, u32[]{:S(2)}, u32[]{:S(2)}) collective-permute-start(bf16[2,9,32,128]{3,2,1,0:T(8,128)(2,1)S(1)} %add_convert_fusion.1), channel_id=1, source_target_pairs={{0,4},{1,9},{2,6},{3,11},{4,0},{5,13},{6,2},{7,15},{8,12},{9,1},{1... | collective-permute-start | bytes 442376 | tf_op jit(solution)/shard_map/ppermute | solution.py:221
  59.2 5.6 %collective-permute-start.26 = (bf16[2,9,32,128]{3,2,1,0:T(8,128)(2,1)S(1)}, bf16[2,9,32,128]{3,2,1,0:T(8,128)(2,1)S(1)}, u32[]{:S(2)}, u32[]{:S(2)}) collective-permute-start(bf16[2,9,32,128]{3,2,1,0:T(8,128)(2,1)S(1)} %get-tuple-element.112), channel_id=1, source_target_pairs={{0,4},{1,9},{2,6},{3,11},{4,0},{5,13},{6,2},{7,15},{8,12},{9,1},{1... | collective-permute-start | bytes 442376 | tf_op jit(solution)/shard_map/ppermute | solution.py:221
  60.1 5.1 %collective-permute-start.27 = (bf16[2,9,32,128]{3,2,1,0:T(8,128)(2,1)S(1)}, bf16[2,9,32,128]{3,2,1,0:T(8,128)(2,1)S(1)}, u32[]{:S(2)}, u32[]{:S(2)}) collective-permute-start(bf16[2,9,32,128]{3,2,1,0:T(8,128)(2,1)S(1)} %get-tuple-element.113), channel_id=1, source_target_pairs={{0,8},{1,3},{2,10},{3,1},{4,12},{5,7},{6,14},{7,5},{8,0},{9,11},{1... | collective-permute-start | bytes 442376 | tf_op jit(solution)/shard_map/ppermute | solution.py:221
  63.1 5.2 %collective-permute-start.25 = (bf16[2,9,32,128]{3,2,1,0:T(8,128)(2,1)S(1)}, bf16[2,9,32,128]{3,2,1,0:T(8,128)(2,1)S(1)}, u32[]{:S(2)}, u32[]{:S(2)}) collective-permute-start(bf16[2,9,32,128]{3,2,1,0:T(8,128)(2,1)S(1)} %shard_map.102), channel_id=1, source_target_pairs={{0,2},{1,5},{2,0},{3,7},{4,6},{5,1},{6,4},{7,3},{8,10},{9,13},{10,... | collective-permute-start | bytes 442376 | tf_op jit(solution)/shard_map/ppermute | solution.py:221
  68.4 6.1 %collective-permute-start.28 = (bf16[9,32,128]{2,1,0:T(8,128)(2,1)S(1)}, bf16[9,32,128]{2,1,0:T(8,128)(2,1)S(1)}, u32[]{:S(2)}, u32[]{:S(2)}) collective-permute-start(bf16[9,32,128]{2,1,0:T(8,128)(2,1)S(1)} %get-tuple-element.115), channel_id=1, source_target_pairs={{0,16},{1,17},{2,18},{3,19},{4,20},{5,21},{6,22},{7,23},{8,24},{9,... | collective-permute-start | bytes 221192 | tf_op jit(solution)/shard_map/ppermute | solution.py:217
  69.5 1.2 collective-permute-start.7
  69.5 1.3 collective-permute-start.18
  70.9 3.6 %copy-start.6 = (s32[12]{0:T(128)S(1)}, s32[12]{0:T(128)}, u32[]{:S(2)}) copy-start(s32[12]{0:T(128)} %ranks_ref.5) | copy-start | bytes 148
  77.0 5.7 %collective-permute-start.29 = (bf16[9,32,128]{2,1,0:T(8,128)(2,1)S(1)}, bf16[9,32,128]{2,1,0:T(8,128)(2,1)S(1)}, u32[]{:S(2)}, u32[]{:S(2)}) collective-permute-start(bf16[9,32,128]{2,1,0:T(8,128)(2,1)S(1)} %get-tuple-element.117), channel_id=1, source_target_pairs={{0,16},{1,17},{2,18},{3,19},{4,20},{5,21},{6,22},{7,23},{8,24},{9,... | collective-permute-start | bytes 221192 | tf_op jit(solution)/shard_map/ppermute | solution.py:217
  82.7 6.0 %collective-permute-start.32 = (bf16[2,9,32,128]{3,2,1,0:T(8,128)(2,1)S(1)}, bf16[2,9,32,128]{3,2,1,0:T(8,128)(2,1)S(1)}, u32[]{:S(2)}, u32[]{:S(2)}) collective-permute-start(bf16[2,9,32,128]{3,2,1,0:T(8,128)(2,1)S(1)} %pad_maximum_fusion.1.refs_0_), channel_id=1, source_target_pairs={{0,8},{1,3},{2,10},{3,1},{4,12},{5,7},{6,14},{7,5},{8,0},{9,11},{1... | collective-permute-start | bytes 442376 | tf_op jit(solution)/shard_map/ppermute | solution.py:221
  82.8 5.9 %collective-permute-start.31 = (bf16[2,9,32,128]{3,2,1,0:T(8,128)(2,1)S(1)}, bf16[2,9,32,128]{3,2,1,0:T(8,128)(2,1)S(1)}, u32[]{:S(2)}, u32[]{:S(2)}) collective-permute-start(bf16[2,9,32,128]{3,2,1,0:T(8,128)(2,1)S(1)} %pad_maximum_fusion.1.refs_0_), channel_id=1, source_target_pairs={{0,4},{1,9},{2,6},{3,11},{4,0},{5,13},{6,2},{7,15},{8,12},{9,1},{1... | collective-permute-start | bytes 442376 | tf_op jit(solution)/shard_map/ppermute | solution.py:221
  83.4 6.5 %collective-permute-start.30 = (bf16[2,9,32,128]{3,2,1,0:T(8,128)(2,1)S(1)}, bf16[2,9,32,128]{3,2,1,0:T(8,128)(2,1)S(1)}, u32[]{:S(2)}, u32[]{:S(2)}) collective-permute-start(bf16[2,9,32,128]{3,2,1,0:T(8,128)(2,1)S(1)} %pad_maximum_fusion.1.refs_0_), channel_id=1, source_target_pairs={{0,2},{1,5},{2,0},{3,7},{4,6},{5,1},{6,4},{7,3},{8,10},{9,13},{10,... | collective-permute-start | bytes 442376 | tf_op jit(solution)/shard_map/ppermute | solution.py:221
  90.0 6.2 %collective-permute-start.33 = (bf16[2,9,32,128]{3,2,1,0:T(8,128)(2,1)S(1)}, bf16[2,9,32,128]{3,2,1,0:T(8,128)(2,1)S(1)}, u32[]{:S(2)}, u32[]{:S(2)}) collective-permute-start(bf16[2,9,32,128]{3,2,1,0:T(8,128)(2,1)S(1)} %collective-permute-done.30.refs_1_), channel_id=1, source_target_pairs={{0,4},{1,9},{2,6},{3,11},{4,0},{5,13},{6,2},{7,15},{8,12},{9,1},{1... | collective-permute-start | bytes 442376 | tf_op jit(solution)/shard_map/ppermute | solution.py:221
  91.4 5.2 %collective-permute-start.35 = (bf16[2,9,32,128]{3,2,1,0:T(8,128)(2,1)S(1)}, bf16[2,9,32,128]{3,2,1,0:T(8,128)(2,1)S(1)}, u32[]{:S(2)}, u32[]{:S(2)}) collective-permute-start(bf16[2,9,32,128]{3,2,1,0:T(8,128)(2,1)S(1)} %collective-permute-done.31.refs_2_), channel_id=1, source_target_pairs={{0,8},{1,3},{2,10},{3,1},{4,12},{5,7},{6,14},{7,5},{8,0},{9,11},{1... | collective-permute-start | bytes 442376 | tf_op jit(solution)/shard_map/ppermute | solution.py:221
  93.5 5.1 %collective-permute-start.34 = (bf16[2,9,32,128]{3,2,1,0:T(8,128)(2,1)S(1)}, bf16[2,9,32,128]{3,2,1,0:T(8,128)(2,1)S(1)}, u32[]{:S(2)}, u32[]{:S(2)}) collective-permute-start(bf16[2,9,32,128]{3,2,1,0:T(8,128)(2,1)S(1)} %collective-permute-done.32.refs_4_), channel_id=1, source_target_pairs={{0,2},{1,5},{2,0},{3,7},{4,6},{5,1},{6,4},{7,3},{8,10},{9,13},{10,... | collective-permute-start | bytes 442376 | tf_op jit(solution)/shard_map/ppermute | solution.py:221
  98.6 6.2 %collective-permute-start.38 = (bf16[2,9,32,128]{3,2,1,0:T(8,128)(2,1)S(1)}, bf16[2,9,32,128]{3,2,1,0:T(8,128)(2,1)S(1)}, u32[]{:S(2)}, u32[]{:S(2)}) collective-permute-start(bf16[2,9,32,128]{3,2,1,0:T(8,128)(2,1)S(1)} %pad_maximum_fusion.1.refs_0_), channel_id=1, source_target_pairs={{0,1},{1,0},{2,3},{3,2},{4,5},{5,4},{6,7},{7,6},{8,9},{9,8},{10,11... | collective-permute-start | bytes 442376 | tf_op jit(solution)/shard_map/ppermute | solution.py:226
  98.6 6.7 %collective-permute-start.39 = (bf16[2,9,32,128]{3,2,1,0:T(8,128)(2,1)S(1)}, bf16[2,9,32,128]{3,2,1,0:T(8,128)(2,1)S(1)}, u32[]{:S(2)}, u32[]{:S(2)}) collective-permute-start(bf16[2,9,32,128]{3,2,1,0:T(8,128)(2,1)S(1)} %collective-permute-done.30.refs_1_), channel_id=1, source_target_pairs={{0,1},{1,0},{2,3},{3,2},{4,5},{5,4},{6,7},{7,6},{8,9},{9,8},{10,11... | collective-permute-start | bytes 442376 | tf_op jit(solution)/shard_map/ppermute | solution.py:226
  99.1 6.2 %collective-permute-start.40 = (bf16[2,9,32,128]{3,2,1,0:T(8,128)(2,1)S(1)}, bf16[2,9,32,128]{3,2,1,0:T(8,128)(2,1)S(1)}, u32[]{:S(2)}, u32[]{:S(2)}) collective-permute-start(bf16[2,9,32,128]{3,2,1,0:T(8,128)(2,1)S(1)} %collective-permute-done.31.refs_2_), channel_id=1, source_target_pairs={{0,1},{1,0},{2,3},{3,2},{4,5},{5,4},{6,7},{7,6},{8,9},{9,8},{10,11... | collective-permute-start | bytes 442376 | tf_op jit(solution)/shard_map/ppermute | solution.py:226
  99.2 6.7 %collective-permute-start.42 = (bf16[2,9,32,128]{3,2,1,0:T(8,128)(2,1)S(1)}, bf16[2,9,32,128]{3,2,1,0:T(8,128)(2,1)S(1)}, u32[]{:S(2)}, u32[]{:S(2)}) collective-permute-start(bf16[2,9,32,128]{3,2,1,0:T(8,128)(2,1)S(1)} %collective-permute-done.32.refs_4_), channel_id=1, source_target_pairs={{0,1},{1,0},{2,3},{3,2},{4,5},{5,4},{6,7},{7,6},{8,9},{9,8},{10,11... | collective-permute-start | bytes 442376 | tf_op jit(solution)/shard_map/ppermute | solution.py:226
  99.7 5.1 %collective-permute-start.37 = (bf16[2,9,32,128]{3,2,1,0:T(8,128)(2,1)S(1)}, bf16[2,9,32,128]{3,2,1,0:T(8,128)(2,1)S(1)}, u32[]{:S(2)}, u32[]{:S(2)}) collective-permute-start(bf16[2,9,32,128]{3,2,1,0:T(8,128)(2,1)S(1)} %collective-permute-done.33.refs_3_), channel_id=1, source_target_pairs={{0,8},{1,3},{2,10},{3,1},{4,12},{5,7},{6,14},{7,5},{8,0},{9,11},{1... | collective-permute-start | bytes 442376 | tf_op jit(solution)/shard_map/ppermute | solution.py:221
  104.8 2.3 %collective-permute-start.41 = (bf16[2,9,32,128]{3,2,1,0:T(8,128)(2,1)S(1)}, bf16[2,9,32,128]{3,2,1,0:T(8,128)(2,1)S(1)}, u32[]{:S(2)}, u32[]{:S(2)}) collective-permute-start(bf16[2,9,32,128]{3,2,1,0:T(8,128)(2,1)S(1)} %collective-permute-done.33.refs_3_), channel_id=1, source_target_pairs={{0,1},{1,0},{2,3},{3,2},{4,5},{5,4},{6,7},{7,6},{8,9},{9,8},{10,11... | collective-permute-start | bytes 442376 | tf_op jit(solution)/shard_map/ppermute | solution.py:226
  104.8 2.3 %collective-permute-start.43 = (bf16[2,9,32,128]{3,2,1,0:T(8,128)(2,1)S(1)}, bf16[2,9,32,128]{3,2,1,0:T(8,128)(2,1)S(1)}, u32[]{:S(2)}, u32[]{:S(2)}) collective-permute-start(bf16[2,9,32,128]{3,2,1,0:T(8,128)(2,1)S(1)} %collective-permute-done.34.refs_5_), channel_id=1, source_target_pairs={{0,1},{1,0},{2,3},{3,2},{4,5},{5,4},{6,7},{7,6},{8,9},{9,8},{10,11... | collective-permute-start | bytes 442376 | tf_op jit(solution)/shard_map/ppermute | solution.py:226
  105.3 1.8 %collective-permute-start.44 = (bf16[2,9,32,128]{3,2,1,0:T(8,128)(2,1)S(1)}, bf16[2,9,32,128]{3,2,1,0:T(8,128)(2,1)S(1)}, u32[]{:S(2)}, u32[]{:S(2)}) collective-permute-start(bf16[2,9,32,128]{3,2,1,0:T(8,128)(2,1)S(1)} %collective-permute-done.35.refs_6_), channel_id=1, source_target_pairs={{0,1},{1,0},{2,3},{3,2},{4,5},{5,4},{6,7},{7,6},{8,9},{9,8},{10,11... | collective-permute-start | bytes 442376 | tf_op jit(solution)/shard_map/ppermute | solution.py:226
  105.4 1.8 %collective-permute-start.45 = (bf16[2,9,32,128]{3,2,1,0:T(8,128)(2,1)S(1)}, bf16[2,9,32,128]{3,2,1,0:T(8,128)(2,1)S(1)}, u32[]{:S(2)}, u32[]{:S(2)}) collective-permute-start(bf16[2,9,32,128]{3,2,1,0:T(8,128)(2,1)S(1)} %collective-permute-done.37.refs_7_), channel_id=1, source_target_pairs={{0,1},{1,0},{2,3},{3,2},{4,5},{5,4},{6,7},{7,6},{8,9},{9,8},{10,11... | collective-permute-start | bytes 442376 | tf_op jit(solution)/shard_map/ppermute | solution.py:226
  105.8 6.7 %collective-permute-start.46 = (bf16[1,32,256]{2,1,0:T(8,128)(2,1)S(1)}, bf16[1,32,256]{2,1,0:T(8,128)(2,1)S(1)}, u32[]{:S(2)}, u32[]{:S(2)}) collective-permute-start(bf16[1,32,256]{2,1,0:T(8,128)(2,1)S(1)} %get-tuple-element.136), channel_id=1, source_target_pairs={{1,3},{3,5},{5,7},{7,9},{9,11},{11,13},{13,15},{15,17},{17,19},{19... | collective-permute-start | bytes 49160 | tf_op jit(solution)/shard_map/ppermute | solution.py:341
  112.5 3.3 %collective-permute-start.49 = (bf16[4,2,9,32,128]{4,3,2,1,0:T(8,128)(2,1)S(1)}, bf16[4,2,9,32,128]{4,3,2,1,0:T(8,128)(2,1)S(1)}, u32[]{:S(2)}, u32[]{:S(2)}) collective-permute-start(bf16[4,2,9,32,128]{4,3,2,1,0:T(8,128)(2,1)S(1)} %get-tuple-element.141), channel_id=1, source_target_pairs={{0,1},{1,0},{2,3},{3,2},{4,5},{5,4},{6,7},{7,6},{8,9},{9,8},{10,11... | collective-permute-start | bytes 1769480 | tf_op jit(solution)/shard_map/ppermute | solution.py:226
  114.2 11.5 %collective-permute-start.48 = (bf16[4,2,9,32,128]{4,3,2,1,0:T(8,128)(2,1)S(1)}, bf16[4,2,9,32,128]{4,3,2,1,0:T(8,128)(2,1)S(1)}, u32[]{:S(2)}, u32[]{:S(2)}) collective-permute-start(bf16[4,2,9,32,128]{4,3,2,1,0:T(8,128)(2,1)S(1)} %get-tuple-element.139), channel_id=1, source_target_pairs={{0,1},{1,0},{2,3},{3,2},{4,5},{5,4},{6,7},{7,6},{8,9},{9,8},{10,11... | collective-permute-start | bytes 1769480 | tf_op jit(solution)/shard_map/ppermute | solution.py:226
  116.0 7.1 %collective-permute-start.50 = (bf16[2,9,32,128]{3,2,1,0:T(8,128)(2,1)S(1)}, bf16[2,9,32,128]{3,2,1,0:T(8,128)(2,1)S(1)}, u32[]{:S(2)}, u32[]{:S(2)}) collective-permute-start(bf16[2,9,32,128]{3,2,1,0:T(8,128)(2,1)S(1)} %get-tuple-element.142), channel_id=1, source_target_pairs={{0,8},{1,3},{2,10},{3,1},{4,12},{5,7},{6,14},{7,5},{8,0},{9,11},{1... | collective-permute-start | bytes 442376 | tf_op jit(solution)/shard_map/ppermute | solution.py:221
  118.4 5.7 %collective-permute-start.51 = (bf16[2,9,32,128]{3,2,1,0:T(8,128)(2,1)S(1)}, bf16[2,9,32,128]{3,2,1,0:T(8,128)(2,1)S(1)}, u32[]{:S(2)}, u32[]{:S(2)}) collective-permute-start(bf16[2,9,32,128]{3,2,1,0:T(8,128)(2,1)S(1)} %get-tuple-element.143), channel_id=1, source_target_pairs={{0,4},{1,9},{2,6},{3,11},{4,0},{5,13},{6,2},{7,15},{8,12},{9,1},{1... | collective-permute-start | bytes 442376 | tf_op jit(solution)/shard_map/ppermute | solution.py:221
  118.4 5.7 %collective-permute-start.52 = (bf16[2,9,32,128]{3,2,1,0:T(8,128)(2,1)S(1)}, bf16[2,9,32,128]{3,2,1,0:T(8,128)(2,1)S(1)}, u32[]{:S(2)}, u32[]{:S(2)}) collective-permute-start(bf16[2,9,32,128]{3,2,1,0:T(8,128)(2,1)S(1)} %get-tuple-element.144), channel_id=1, source_target_pairs={{0,2},{1,5},{2,0},{3,7},{4,6},{5,1},{6,4},{7,3},{8,10},{9,13},{10,... | collective-permute-start | bytes 442376 | tf_op jit(solution)/shard_map/ppermute | solution.py:221
  124.1 5.2 %collective-permute-start.53 = (bf16[2,9,32,128]{3,2,1,0:T(8,128)(2,1)S(1)}, bf16[2,9,32,128]{3,2,1,0:T(8,128)(2,1)S(1)}, u32[]{:S(2)}, u32[]{:S(2)}) collective-permute-start(bf16[2,9,32,128]{3,2,1,0:T(8,128)(2,1)S(1)} %add_convert_fusion), channel_id=1, source_target_pairs={{0,4},{1,9},{2,6},{3,11},{4,0},{5,13},{6,2},{7,15},{8,12},{9,1},{1... | collective-permute-start | bytes 442376 | tf_op jit(solution)/shard_map/ppermute | solution.py:221
  125.8 6.3 %collective-permute-start.55 = (bf16[2,9,32,128]{3,2,1,0:T(8,128)(2,1)S(1)}, bf16[2,9,32,128]{3,2,1,0:T(8,128)(2,1)S(1)}, u32[]{:S(2)}, u32[]{:S(2)}) collective-permute-start(bf16[2,9,32,128]{3,2,1,0:T(8,128)(2,1)S(1)} %get-tuple-element.150), channel_id=1, source_target_pairs={{0,4},{1,9},{2,6},{3,11},{4,0},{5,13},{6,2},{7,15},{8,12},{9,1},{1... | collective-permute-start | bytes 442376 | tf_op jit(solution)/shard_map/ppermute | solution.py:221
  126.4 5.7 %collective-permute-start.56 = (bf16[2,9,32,128]{3,2,1,0:T(8,128)(2,1)S(1)}, bf16[2,9,32,128]{3,2,1,0:T(8,128)(2,1)S(1)}, u32[]{:S(2)}, u32[]{:S(2)}) collective-permute-start(bf16[2,9,32,128]{3,2,1,0:T(8,128)(2,1)S(1)} %get-tuple-element.151), channel_id=1, source_target_pairs={{0,8},{1,3},{2,10},{3,1},{4,12},{5,7},{6,14},{7,5},{8,0},{9,11},{1... | collective-permute-start | bytes 442376 | tf_op jit(solution)/shard_map/ppermute | solution.py:221
  129.4 5.2 %collective-permute-start.54 = (bf16[2,9,32,128]{3,2,1,0:T(8,128)(2,1)S(1)}, bf16[2,9,32,128]{3,2,1,0:T(8,128)(2,1)S(1)}, u32[]{:S(2)}, u32[]{:S(2)}) collective-permute-start(bf16[2,9,32,128]{3,2,1,0:T(8,128)(2,1)S(1)} %shard_map.110), channel_id=1, source_target_pairs={{0,2},{1,5},{2,0},{3,7},{4,6},{5,1},{6,4},{7,3},{8,10},{9,13},{10,... | collective-permute-start | bytes 442376 | tf_op jit(solution)/shard_map/ppermute | solution.py:221
  134.7 6.1 %collective-permute-start.57 = (bf16[9,32,128]{2,1,0:T(8,128)(2,1)S(1)}, bf16[9,32,128]{2,1,0:T(8,128)(2,1)S(1)}, u32[]{:S(2)}, u32[]{:S(2)}) collective-permute-start(bf16[9,32,128]{2,1,0:T(8,128)(2,1)S(1)} %get-tuple-element.153), channel_id=1, source_target_pairs={{0,16},{1,17},{2,18},{3,19},{4,20},{5,21},{6,22},{7,23},{8,24},{9,... | collective-permute-start | bytes 221192 | tf_op jit(solution)/shard_map/ppermute | solution.py:217
  135.0 1.2 collective-permute-start.36
  135.0 1.3 collective-permute-start.47
  (4 other events, 9.0 us)

commit v9 on v8

--- a/solution.py
+++ b/solution.py
@@ -69,10 +69,20 @@
     return copies
 
 
-def coeff_kernel(ranks_ref, v_hbm, basis_hbm, transfer_hbm, out_ref, v_ref, basis_ref, transfer_ref, sems):
+def emit_edges(core_ref, v_ref, inner_ref, outer_ref):
+    head, tail = v_ref[0], v_ref[v_ref.shape[0] - 1]
+    even = core_ref[0] == 0
+    inner_ref[0] = jnp.where(even, tail, head)
+    outer_ref[0] = jnp.where(even, head, tail)
+
+
+def coeff_kernel(
+    ranks_ref, core_ref, v_hbm, basis_hbm, transfer_hbm, out_ref, inner_ref, outer_ref, v_ref, basis_ref, transfer_ref, sems
+):
     leaves, rank_top, _ = basis_ref.shape
     for copy in fetch([(v_hbm, v_ref), (basis_hbm, basis_ref), (transfer_hbm, transfer_ref)], sems):
         copy.wait()
+    emit_edges(core_ref, v_ref, inner_ref, outer_ref)
     emit_coeffs(lambda i: v_ref[i], basis_ref, transfer_ref, ranks_ref, out_ref, leaves, rank_top)
 
 
@@ -141,34 +151,25 @@
     out_ref[1] = dot(jnp.where(even, inner, outer), last_ref[0, 0])
 
 
-def first_add_kernel(keep_ref, swap_ref, *out_refs):
+def add_kernel(keep_ref, swap_ref, *out_refs):
     for n, out_ref in enumerate(out_refs):
-        out_ref[...] = (keep_ref[n].astype(F32) + swap_ref[n].astype(F32)).astype(BF)
-
-
-def second_add_kernel(keep_ref, swap_ref, yz_ref, zx_ref, own_out, y_out, z_out):
-    own_out[...] = keep_ref[0].astype(F32) + swap_ref[0].astype(F32)
-    y_out[...] = (keep_ref[2].astype(F32) + swap_ref[2].astype(F32)).astype(BF)
-    total = keep_ref[3].astype(F32) + swap_ref[3].astype(F32)
-    z_out[...] = (total + yz_ref[...].astype(F32) + zx_ref[...].astype(F32)).astype(BF)
-
-
-def third_add_kernel(keep_ref, swap_ref, x_ref, x_out):
-    total = keep_ref[1].astype(F32) + swap_ref[1].astype(F32) + x_ref[...].astype(F32)
-    x_out[...] = total.astype(BF)
-
-
-def last_add_kernel(own_ref, x_ref, y_ref, z_ref, keep_out, *away_refs):
+        out_ref[...] = (keep_ref[n].astype(F32) + swap_ref[n].astype(F32)).astype(out_ref.dtype)
+
+
+def last_add_kernel(own_ref, *refs, parts):
+    part_refs, (keep_out, *away_refs) = refs[:parts], refs[parts:]
     for f in range(own_ref.shape[0]):
-        total = own_ref[f] + x_ref[f].astype(F32) + y_ref[f].astype(F32) + z_ref[f].astype(F32)
+        total = own_ref[f]
+        for part_ref in part_refs:
+            total = total + part_ref[f].astype(F32)
         if f == 0:
             keep_out[...] = total
         else:
             away_refs[f - 1][...] = total.astype(BF)
 
 
-def field_kernel(ranks_ref, near_ref, edge_ref, basis_ref, transfer_ref, keep_ref, *rest, away):
-    term_refs, out_ref, coeff_ref = rest[:away], rest[away], rest[away + 1 :]
+def field_kernel(ranks_ref, core_ref, near_ref, edge_ref, basis_ref, transfer_ref, keep_ref, *rest, away):
+    term_refs, out_ref, next_refs = rest[:away], rest[away], rest[away + 1 :]
     leaves, rank_top, _ = basis_ref.shape
     mains, rhs, _ = keep_ref.shape
     tiles = []
@@ -191,8 +192,10 @@
         if i == leaves - 1:
             result = result + edge_ref[1]
         out_ref[i] = result.astype(BF)
-    if coeff_ref:
-        emit_coeffs(lambda i: out_ref[i], basis_ref, transfer_ref, ranks_ref, coeff_ref[0], leaves, rank_top)
+    if next_refs:
+        coeff_ref, inner_ref, outer_ref = next_refs
+        emit_edges(core_ref, out_ref, inner_ref, outer_ref)
+        emit_coeffs(lambda i: out_ref[i], basis_ref, transfer_ref, ranks_ref, coeff_ref, leaves, rank_top)
 
 
 def params(mebibytes):
@@ -226,6 +229,8 @@
         return lax.ppermute(part, "clu", [(d, d ^ 1) for d in range(devices)])
 
     me = lax.axis_index("clu")
+    core = me % cores
+    barrier = lax.optimization_barrier
 
     def rows(cluster, sign):
         device = cluster // clusters
@@ -241,18 +246,20 @@
     out_shape = shape((leaves, rhs, width), BF)
     tile_out = shape(tile_shape, BF)
     part_shape = shape((far,) + tile_shape, BF)
-    first_coeffs = pl.pallas_call(
+    edge_shape = shape((1, rhs, width), BF)
+    core_index = core.reshape(1)
+    first_coeffs, inner, outer = pl.pallas_call(
         coeff_kernel,
-        out_shape=tile_out,
-        in_specs=[SMEM, HBM, HBM, HBM],
-        out_specs=VMEM,
+        out_shape=[tile_out, edge_shape, edge_shape],
+        in_specs=[SMEM, SMEM, HBM, HBM, HBM],
+        out_specs=[VMEM] * 3,
         scratch_shapes=[
             pltpu.VMEM(charges.shape, BF),
             pltpu.VMEM(basis.shape, BF),
             pltpu.VMEM(transfer.shape, BF),
             pltpu.SemaphoreType.DMA((3,)),
         ],
-    )(ranks, charges, basis, transfer)
+    )(ranks, core_index, charges, basis, transfer)
 
     order = ((x | y | z, x | y, y | z, z | x), (0, x, y, z))
     couple = pl.pallas_call(
@@ -306,59 +313,53 @@
         )
 
     own_shape = shape((far,) + tile_shape, F32)
-    first_add = adder(first_add_kernel, 2, [part_shape] * 4)
-    second_add = adder(second_add_kernel, 4, [own_shape, part_shape, part_shape])
-    third_add = adder(third_add_kernel, 3, [part_shape])
-    last_add = adder(last_add_kernel, 4, [shape(tile_shape, F32)] + [tile_out] * (far - 1))
+    far_add = adder(add_kernel, 2, [part_shape] * 4)
+    near_add = adder(add_kernel, 2, [own_shape] + [part_shape] * 3)
+    last_add = adder(
+        functools.partial(last_add_kernel, parts=chips - 1),
+        chips,
+        [shape(tile_shape, F32)] + [tile_out] * (far - 1),
+    )
 
     def finish(with_coeffs):
         return pl.pallas_call(
             functools.partial(field_kernel, away=far - 1),
-            out_shape=[out_shape, tile_out] if with_coeffs else [out_shape],
-            in_specs=[SMEM] + [VMEM] * (4 + far),
-            out_specs=[VMEM, VMEM] if with_coeffs else [VMEM],
+            out_shape=[out_shape, tile_out, edge_shape, edge_shape] if with_coeffs else [out_shape],
+            in_specs=[SMEM, SMEM] + [VMEM] * (4 + far),
+            out_specs=[VMEM] * 4 if with_coeffs else [VMEM],
             compiler_params=params(16),
         )
 
-    core = me % cores
-    barrier = lax.optimization_barrier
-
     halo_pairs = [(d, d + cores) for d in range(1, devices - cores, cores)]
     halo_pairs += [(d, d - cores) for d in range(cores, devices, cores)]
 
-    def apply_matrix(field_in, coeffs, coupling, with_coeffs):
-        head, tail = field_in[:1], field_in[leaves - 1 :]
+    long, short = order[0], order[1][1:]
+
+    def apply_matrix(field_in, coeffs, inner, outer, coupling, with_coeffs):
         away = [swap_far(coeffs, s) for s in range(1, far)]
-        away, coupling = barrier((away, coupling))
-        got = {0: jnp.stack([coeffs] + away)}
-        got[x], got[y], got[z] = barrier((swap(got[0], x), swap(got[0], y), swap(got[0], z)))
+        outer = lax.ppermute(outer, "clu", halo_pairs)
+        away, outer, coupling = barrier((away, outer, coupling))
+        column = jnp.stack([coeffs] + away)
+        got = {chip: swap(column, chip) for chip in long + short}
         near_sum = near(field_in, near_field)
-        got |= {x | y: swap(got[x], y), y | z: swap(got[y], z), z | x: swap(got[z], x)}
         got, near_sum = barrier((got, near_sum))
+        got[0] = column
         other = {chip: swap_cores(got[chip]) for chip in got}
-        got[x | y | z], outer = barrier((swap(got[x | y], z), jnp.where(core == 0, head, tail)))
-        other[x | y | z] = swap_cores(got[x | y | z])
-        outer = lax.ppermute(outer, "clu", halo_pairs)
-        totals = couple(
+        keep_long, keep, send_long, send = couple(
             source_rows,
             target_rows,
             coupling,
             *[got[chip] for chip in range(chips)],
             *[other[chip] for chip in range(chips)],
         )
-        (keep_first, keep, send_first, send), outer = barrier((totals, outer))
-        corner, xy, yz, zx = first_add(keep_first, swap_cores(send_first))
-        swapped = swap_cores(send)
-        inner, outer = swap_cores(jnp.where(core == 0, tail, head)), swap_cores(outer)
-        edges = edge(core.reshape(1), inner, outer, near_field, near_field)
-        corner, yz, zx = barrier((swap(corner, z), swap(yz, y), swap(zx, x)))
-        xy = swap((xy.astype(F32) + corner.astype(F32)).astype(BF), y)
-        mine, to_y, to_z = second_add(keep, swapped, yz, zx)
-        to_y, to_z = swap(to_y, y), swap(to_z, z)
-        (to_x,) = third_add(keep, swapped, xy)
-        total, *away = last_add(mine, swap(to_x, x), to_y, to_z)
+        parts = far_add(keep_long, swap_cores(send_long))
+        own, *rest = near_add(keep, swap_cores(send))
+        parts = [swap(part, chip) for part, chip in zip([*parts, *rest], long + short)]
+        total, *away = last_add(own, *parts)
         terms = [swap_far(part, s + 1) for s, part in enumerate(away)]
-        return finish(with_coeffs)(ranks, near_sum, edges, basis, transfer, total, *terms)
+        inner, outer = swap_cores(inner), swap_cores(outer)
+        edges = edge(core_index, inner, outer, near_field, near_field)
+        return finish(with_coeffs)(ranks, core_index, near_sum, edges, basis, transfer, total, *terms)
 
     coupling, first_coeffs = barrier((coupling, first_coeffs))
     coupling = pl.pallas_call(
@@ -368,8 +369,8 @@
         out_specs=pl.BlockSpec(memory_space=pl.ANY),
         input_output_aliases={0: 0},
     )(coupling)
-    first, second_coeffs = apply_matrix(charges, first_coeffs, coupling, True)
-    (second,) = apply_matrix(first, second_coeffs, coupling, False)
+    first, *second_args = apply_matrix(charges, first_coeffs, inner, outer, coupling, True)
+    (second,) = apply_matrix(first, *second_args, coupling, False)
     return (first, second)
 
 

time: 144 us -> 157 us (1.090)
  starting transfers between devices: 46.5 us -> 60.2 us
  local copies, waits for them, and re-layouts: 6.56 us -> 14.6 us
  waiting for transfers between devices: 66.5 us -> 58.6 us
    ppermute x28, starting transfers between devices: 29.3 us -> 42.8 us  [swap(): lax.ppermute(part, 'clu', [(d, d ^ (turned if d % cores else direction) *...]
    ppermute x28, waiting for transfers between devices: 47.8 us -> 39.1 us  [swap(): lax.ppermute(part, 'clu', [(d, d ^ (turned if d % cores else direction) *...]
    unnamed x20 -> x42, local copies, waits for them, and re-layouts: 1.78 us -> 9.78 us
    ppermute x4, waiting for transfers between devices: 13.1 us -> 6.51 us  [swap_far(): lax.ppermute(part, 'clu', [(d, (d + shift * cube) % devices) for d in ran...]
    ppermute x2, waiting for transfers between devices: 0.01 us -> 5.48 us  [apply_matrix(): outer = lax.ppermute(outer, 'clu', halo_pairs)]
    ppermute x4, starting transfers between devices: 5.9 us -> 9.7 us  [swap_far(): lax.ppermute(part, 'clu', [(d, (d + shift * cube) % devices) for d in ran...]
    ppermute x24, starting transfers between devices: 8.71 us -> 5.15 us  [swap_cores(): return lax.ppermute(part, 'clu', [(d, d ^ 1) for d in range(devices)])]
    ppermute x24, waiting for transfers between devices: 5.69 us -> 7.54 us  [swap_cores(): return lax.ppermute(part, 'clu', [(d, d ^ 1) for d in range(devices)])]
  transfers between devices with their start and end apart: 58 -> 58, of which waited for: 33 -> 31; matrix products, arithmetic and copies ran while one was open for 3% -> 4% of each run, Pallas kernels for 9% -> 1%
where the time goes in v9:
time: 157 us
  starting transfers between devices  60.2 us (38%)
  waiting for transfers between devices  58.6 us (37%)
  Pallas kernels  21.5 us (14%)
  local copies, waits for them, and re-layouts  14.6 us (9%)
    ppermute x28, starting transfers between devices, swap(): lax.ppermute(part, 'clu', [(d, d ^ (turned if d % cores else direction) *...  42.8 us
    ppermute x28, waiting for transfers between devices, swap(): lax.ppermute(part, 'clu', [(d, d ^ (turned if d % cores else direction) *...  39.1 us
    pallas_call x2, Pallas kernels, apply_matrix(): couple(source_rows, target_rows, coupling, *[got[chip] for chip in range(...  11.3 us
    unnamed x42, local copies, waits for them, and re-layouts  9.78 us
    ppermute x4, starting transfers between devices, swap_far(): lax.ppermute(part, 'clu', [(d, (d + shift * cube) % devices) for d in ran...  9.7 us
    ppermute x24, waiting for transfers between devices, swap_cores(): return lax.ppermute(part, 'clu', [(d, d ^ 1) for d in range(devices)])  7.54 us
    ppermute x4, waiting for transfers between devices, swap_far(): lax.ppermute(part, 'clu', [(d, (d + shift * cube) % devices) for d in ran...  6.51 us
    ppermute x2, waiting for transfers between devices, apply_matrix(): outer = lax.ppermute(outer, 'clu', halo_pairs)  5.48 us
  transfers between devices with their start and end apart: 58, of which 31 were waited for; matrix products, arithmetic and copies ran while one was open for 4% of the time, Pallas kernels for 1%

profile of v9, /device:TPU:0, one launch (start us, length us, event | category | flops | bytes accessed | tf_op | source)
XLA Modules:
  0.0 156.6 jit_solution(1342445946246663191)
XLA Ops:
  0.6 2.9 %shard_map.95 = (bf16[9,32,128]{2,1,0:T(8,128)(2,1)}, bf16[1,32,256]{2,1,0:T(8,128)(2,1)}, bf16[1,32,256]{2,1,0:T(8,128)(2,1)}) custom-call(s32[12]{0:T(128)} %ranks_ref.5, s32[1]{0:T(128)} %bitcast.core_ref, bf16[8,32,256]{2,1,0:T(8,128)(2,1)} %v_ref.1, bf16[8,96,256]{2,1,0:T(8,128)(2,1)} %basis_ref.3, bf16[8,96,96]{2,1,0:T(8,128)(2,1)} %transfer_ref.3), custom_call_target="tpu_custom_call" | custom-call | tf_op jit(solution)/shard_map/pallas_call | solution.py:251
  3.5 4.1 %collective-permute-start = (bf16[9,32,128]{2,1,0:T(8,128)(2,1)}, bf16[9,32,128]{2,1,0:T(8,128)(2,1)S(1)}, u32[]{:S(2)}, u32[]{:S(2)}) collective-permute-start(bf16[9,32,128]{2,1,0:T(8,128)(2,1)} %get-tuple-element.62), channel_id=1, source_target_pairs={{0,16},{1,17},{2,18},{3,19},{4,20},{5,21},{6,22},{7,23},{8,24},{9,... | collective-permute-start | bytes 221192 | tf_op jit(solution)/shard_map/ppermute | solution.py:220
  7.6 1.3 collective-permute-start.1
  8.9 4.8 %copy.11.in_ref = bf16[128,96,96]{2,1,0:T(8,128)(2,1)} copy(bf16[128,96,96]{0,2,1:T(8,128)(2,1)} %param.12) | data formatting | bytes 4718592 | tf_op jit(solution)/shard_map/optimization_barrier | solution.py:364
  13.7 0.9 copy-done.17
  14.6 2.7 %collective-permute-start.2 = (bf16[2,9,32,128]{3,2,1,0:T(8,128)(2,1)S(1)}, bf16[2,9,32,128]{3,2,1,0:T(8,128)(2,1)}, u32[]{:S(2)}, u32[]{:S(2)}) collective-permute-start(bf16[2,9,32,128]{3,2,1,0:T(8,128)(2,1)S(1)} %pad_maximum_fusion.refs_0_), channel_id=1, source_target_pairs={{0,2},{1,5},{2,0},{3,7},{4,6},{5,1},{6,4},{7,3},{8,10},{9,13},{10,... | collective-permute-start | bytes 442376 | tf_op jit(solution)/shard_map/ppermute | solution.py:224
  17.3 1.5 collective-permute-start.3
  18.8 0.9 collective-permute-start.4
  19.7 3.0 %collective-permute-start.5 = (bf16[2,9,32,128]{3,2,1,0:T(8,128)(2,1)S(1)}, bf16[2,9,32,128]{3,2,1,0:T(8,128)(2,1)S(1)}, u32[]{:S(2)}, u32[]{:S(2)}) collective-permute-start(bf16[2,9,32,128]{3,2,1,0:T(8,128)(2,1)S(1)} %pad_maximum_fusion.refs_0_), channel_id=1, source_target_pairs={{0,8},{1,3},{2,10},{3,1},{4,12},{5,7},{6,14},{7,5},{8,0},{9,11},{1... | collective-permute-start | bytes 442376 | tf_op jit(solution)/shard_map/ppermute | solution.py:224
  22.7 2.4 %collective-permute-start.7 = (bf16[2,9,32,128]{3,2,1,0:T(8,128)(2,1)S(1)}, bf16[2,9,32,128]{3,2,1,0:T(8,128)(2,1)S(1)}, u32[]{:S(2)}, u32[]{:S(2)}) collective-permute-start(bf16[2,9,32,128]{3,2,1,0:T(8,128)(2,1)S(1)} %pad_maximum_fusion.refs_0_), channel_id=1, source_target_pairs={{0,12},{1,11},{2,14},{3,9},{4,8},{5,15},{6,10},{7,13},{8,4},{9,3},... | collective-permute-start | bytes 442376 | tf_op jit(solution)/shard_map/ppermute | solution.py:224
  25.4 2.7 %collective-permute-start.8 = (bf16[2,9,32,128]{3,2,1,0:T(8,128)(2,1)S(1)}, bf16[2,9,32,128]{3,2,1,0:T(8,128)(2,1)S(1)}, u32[]{:S(2)}, u32[]{:S(2)}) collective-permute-start(bf16[2,9,32,128]{3,2,1,0:T(8,128)(2,1)S(1)} %pad_maximum_fusion.refs_0_), channel_id=1, source_target_pairs={{0,14},{1,15},{2,12},{3,13},{4,10},{5,11},{6,8},{7,9},{8,6},{9,7},... | collective-permute-start | bytes 442376 | tf_op jit(solution)/shard_map/ppermute | solution.py:224
  28.1 0.9 copy-done.4
  29.6 1.9 %collective-permute-done.4.refs_3_ = bf16[2,9,32,128]{3,2,1,0:T(8,128)(2,1)S(1)} collective-permute-done((bf16[2,9,32,128]{3,2,1,0:T(8,128)(2,1)S(1)}, bf16[2,9,32,128]{3,2,1,0:T(8,128)(2,1)S(1)}, u32[]{:S(2)}, u32[]{:S(2)}) %collective-permute-start.4) | collective-permute-done | bytes 147488 | tf_op jit(solution)/shard_map/ppermute | solution.py:224
  31.5 2.8 %collective-permute-done.7.refs_6_ = bf16[2,9,32,128]{3,2,1,0:T(8,128)(2,1)S(1)} collective-permute-done((bf16[2,9,32,128]{3,2,1,0:T(8,128)(2,1)S(1)}, bf16[2,9,32,128]{3,2,1,0:T(8,128)(2,1)S(1)}, u32[]{:S(2)}, u32[]{:S(2)}) %collective-permute-start.7) | collective-permute-done | bytes 147488 | tf_op jit(solution)/shard_map/ppermute | solution.py:224
  34.3 1.2 collective-permute-done.8.refs_7_
  35.5 0.6 copy-done.13
  37.3 0.7 collective-permute-done.13.refs_10_
  38.2 0.7 fusion.1
  38.9 0.7 collective-permute-done.18.refs_15_
  39.6 1.9 %copy-done.1 = bf16[128,96,96]{2,1,0:T(8,128)(2,1)S(1)} copy-done((bf16[128,96,96]{2,1,0:T(8,128)(2,1)S(1)}, bf16[128,96,96]{2,1,0:T(8,128)(2,1)}, u32[]{:S(2)}) %copy-start.1) | copy-done | bytes 2359320
  41.5 0.9 copy-done.6
  42.4 0.9 copy-done.8
  43.3 0.9 copy-done.10
  44.2 0.9 copy-done.12
  45.2 0.9 copy-done.14
  46.1 6.0 %shard_map.99 = (bf16[4,2,9,32,128]{4,3,2,1,0:T(8,128)(2,1)S(1)}, bf16[4,2,9,32,128]{4,3,2,1,0:T(8,128)(2,1)S(1)}, bf16[4,2,9,32,128]{4,3,2,1,0:T(8,128)(2,1)S(1)}, bf16[4,2,9,32,128]{4,3,2,1,0:T(8,128)(2,1)S(1)}) custom-call(s32[128]{0:T(128)S(1)} %get-tuple-element.120.source_ref, s32[128]{0:T(128)S(1)} %get-tuple-element.121.target_ref, ...), custom_call_target="tpu_custom_call" | custom-call | flops 75497472 | bytes 10485760 | tf_op jit(solution)/shard_map/pallas_call | solution.py:348
  52.7 1.5 collective-permute-done.20.swap_ref
  54.3 2.0 %collective-permute-start.21 = (bf16[2,9,32,128]{3,2,1,0:T(8,128)(2,1)S(1)}, bf16[2,9,32,128]{3,2,1,0:T(8,128)(2,1)S(1)}, u32[]{:S(2)}, u32[]{:S(2)}) collective-permute-start(bf16[2,9,32,128]{3,2,1,0:T(8,128)(2,1)S(1)} %get-tuple-element.82), channel_id=1, source_target_pairs={{0,14},{1,15},{2,12},{3,13},{4,10},{5,11},{6,8},{7,9},{8,6},{9,7},... | collective-permute-start | bytes 442376 | tf_op jit(solution)/shard_map/ppermute | solution.py:224
  56.3 2.0 %collective-permute-start.22 = (bf16[2,9,32,128]{3,2,1,0:T(8,128)(2,1)S(1)}, bf16[2,9,32,128]{3,2,1,0:T(8,128)(2,1)S(1)}, u32[]{:S(2)}, u32[]{:S(2)}) collective-permute-start(bf16[2,9,32,128]{3,2,1,0:T(8,128)(2,1)S(1)} %get-tuple-element.83), channel_id=1, source_target_pairs={{0,6},{1,13},{2,4},{3,15},{4,2},{5,9},{6,0},{7,11},{8,14},{9,5},{1... | collective-permute-start | bytes 442376 | tf_op jit(solution)/shard_map/ppermute | solution.py:224
  58.3 2.4 %collective-permute-start.24 = (bf16[2,9,32,128]{3,2,1,0:T(8,128)(2,1)S(1)}, bf16[2,9,32,128]{3,2,1,0:T(8,128)(2,1)S(1)}, u32[]{:S(2)}, u32[]{:S(2)}) collective-permute-start(bf16[2,9,32,128]{3,2,1,0:T(8,128)(2,1)S(1)} %get-tuple-element.85), channel_id=1, source_target_pairs={{0,10},{1,7},{2,8},{3,5},{4,14},{5,3},{6,12},{7,1},{8,2},{9,15},{1... | collective-permute-start | bytes 442376 | tf_op jit(solution)/shard_map/ppermute | solution.py:224
  60.8 2.4 %collective-permute-start.25 = (bf16[2,9,32,128]{3,2,1,0:T(8,128)(2,1)S(1)}, bf16[2,9,32,128]{3,2,1,0:T(8,128)(2,1)S(1)}, u32[]{:S(2)}, u32[]{:S(2)}) collective-permute-start(bf16[2,9,32,128]{3,2,1,0:T(8,128)(2,1)S(1)} %get-tuple-element.86), channel_id=1, source_target_pairs={{0,2},{1,5},{2,0},{3,7},{4,6},{5,1},{6,4},{7,3},{8,10},{9,13},{10,... | collective-permute-start | bytes 442376 | tf_op jit(solution)/shard_map/ppermute | solution.py:224
  63.7 5.7 %collective-permute-done.22.refs_1_ = bf16[2,9,32,128]{3,2,1,0:T(8,128)(2,1)S(1)} collective-permute-done((bf16[2,9,32,128]{3,2,1,0:T(8,128)(2,1)S(1)}, bf16[2,9,32,128]{3,2,1,0:T(8,128)(2,1)S(1)}, u32[]{:S(2)}, u32[]{:S(2)}) %collective-permute-start.22) | collective-permute-done | bytes 147488 | tf_op jit(solution)/shard_map/ppermute | solution.py:224
  69.3 2.0 %collective-permute-start.27 = (bf16[2,9,32,128]{3,2,1,0:T(8,128)(2,1)S(1)}, bf16[2,9,32,128]{3,2,1,0:T(8,128)(2,1)S(1)}, u32[]{:S(2)}, u32[]{:S(2)}) collective-permute-start(bf16[2,9,32,128]{3,2,1,0:T(8,128)(2,1)S(1)} %get-tuple-element.88), channel_id=1, source_target_pairs={{0,8},{1,3},{2,10},{3,1},{4,12},{5,7},{6,14},{7,5},{8,0},{9,11},{1... | collective-permute-start | bytes 442376 | tf_op jit(solution)/shard_map/ppermute | solution.py:224
  71.5 3.0 %collective-permute-done.27.refs_6_ = bf16[2,9,32,128]{3,2,1,0:T(8,128)(2,1)S(1)} collective-permute-done((bf16[2,9,32,128]{3,2,1,0:T(8,128)(2,1)S(1)}, bf16[2,9,32,128]{3,2,1,0:T(8,128)(2,1)S(1)}, u32[]{:S(2)}, u32[]{:S(2)}) %collective-permute-start.27) | collective-permute-done | bytes 147488 | tf_op jit(solution)/shard_map/ppermute | solution.py:224
  74.7 3.9 %collective-permute-start.28 = (bf16[9,32,128]{2,1,0:T(8,128)(2,1)S(1)}, bf16[9,32,128]{2,1,0:T(8,128)(2,1)S(1)}, u32[]{:S(2)}, u32[]{:S(2)}) collective-permute-start(bf16[9,32,128]{2,1,0:T(8,128)(2,1)S(1)} %get-tuple-element.90), channel_id=1, source_target_pairs={{0,16},{1,17},{2,18},{3,19},{4,20},{5,21},{6,22},{7,23},{8,24},{9,... | collective-permute-start | bytes 221192 | tf_op jit(solution)/shard_map/ppermute | solution.py:220
  79.1 0.7 collective-permute-done.9.inner_ref
  80.1 2.1 %collective-permute-done.28.rest_0_ = bf16[9,32,128]{2,1,0:T(8,128)(2,1)S(1)} collective-permute-done((bf16[9,32,128]{2,1,0:T(8,128)(2,1)S(1)}, bf16[9,32,128]{2,1,0:T(8,128)(2,1)S(1)}, u32[]{:S(2)}, u32[]{:S(2)}) %collective-permute-start.28) | collective-permute-done | bytes 73760 | tf_op jit(solution)/shard_map/ppermute | solution.py:220
  82.3 2.5 %shard_map.103 = (bf16[8,32,256]{2,1,0:T(8,128)(2,1)}, bf16[9,32,128]{2,1,0:T(8,128)(2,1)S(1)}, bf16[1,32,256]{2,1,0:T(8,128)(2,1)S(1)}, bf16[1,32,256]{2,1,0:T(8,128)(2,1)S(1)}) custom-call(s32[12]{0:T(128)S(1)} %copy-done.16, s32[1]{0:T(128)} %bitcast.core_ref, f32[8,32,256]{2,1,0:T(8,128)S(1)} %shard_map.97.near_ref, ...), custom_call_target="tpu_custom_call" | custom-call | tf_op jit(solution)/shard_map/pallas_call | solution.py:362
  84.8 1.6 %collective-permute-start.29 = (bf16[9,32,128]{2,1,0:T(8,128)(2,1)S(1)}, bf16[9,32,128]{2,1,0:T(8,128)(2,1)S(1)}, u32[]{:S(2)}, u32[]{:S(2)}) collective-permute-start(bf16[9,32,128]{2,1,0:T(8,128)(2,1)S(1)} %get-tuple-element.92), channel_id=1, source_target_pairs={{0,16},{1,17},{2,18},{3,19},{4,20},{5,21},{6,22},{7,23},{8,24},{9,... | collective-permute-start | bytes 221192 | tf_op jit(solution)/shard_map/ppermute | solution.py:220
  86.4 1.3 collective-permute-start.30
  87.7 5.5 %collective-permute-done.30 = bf16[1,32,256]{2,1,0:T(8,128)(2,1)S(1)} collective-permute-done((bf16[1,32,256]{2,1,0:T(8,128)(2,1)S(1)}, bf16[1,32,256]{2,1,0:T(8,128)(2,1)S(1)}, u32[]{:S(2)}, u32[]{:S(2)}) %collective-permute-start.30) | collective-permute-done | bytes 16416 | tf_op jit(solution)/shard_map/ppermute | solution.py:340
  93.2 3.0 %collective-permute-start.31 = (bf16[2,9,32,128]{3,2,1,0:T(8,128)(2,1)S(1)}, bf16[2,9,32,128]{3,2,1,0:T(8,128)(2,1)S(1)}, u32[]{:S(2)}, u32[]{:S(2)}) collective-permute-start(bf16[2,9,32,128]{3,2,1,0:T(8,128)(2,1)S(1)} %pad_maximum_fusion.1.refs_0_), channel_id=1, source_target_pairs={{0,2},{1,5},{2,0},{3,7},{4,6},{5,1},{6,4},{7,3},{8,10},{9,13},{10,... | collective-permute-start | bytes 442376 | tf_op jit(solution)/shard_map/ppermute | solution.py:224
  96.2 1.5 collective-permute-start.33
  97.7 1.3 collective-permute-start.34
  99.0 2.1 %collective-permute-start.35 = (bf16[2,9,32,128]{3,2,1,0:T(8,128)(2,1)S(1)}, bf16[2,9,32,128]{3,2,1,0:T(8,128)(2,1)S(1)}, u32[]{:S(2)}, u32[]{:S(2)}) collective-permute-start(bf16[2,9,32,128]{3,2,1,0:T(8,128)(2,1)S(1)} %pad_maximum_fusion.1.refs_0_), channel_id=1, source_target_pairs={{0,10},{1,7},{2,8},{3,5},{4,14},{5,3},{6,12},{7,1},{8,2},{9,15},{1... | collective-permute-start | bytes 442376 | tf_op jit(solution)/shard_map/ppermute | solution.py:224
  101.1 2.8 %collective-permute-done.31.refs_1_ = bf16[2,9,32,128]{3,2,1,0:T(8,128)(2,1)S(1)} collective-permute-done((bf16[2,9,32,128]{3,2,1,0:T(8,128)(2,1)S(1)}, bf16[2,9,32,128]{3,2,1,0:T(8,128)(2,1)S(1)}, u32[]{:S(2)}, u32[]{:S(2)}) %collective-permute-start.31) | collective-permute-done | bytes 147488 | tf_op jit(solution)/shard_map/ppermute | solution.py:224
  104.0 4.2 %collective-permute-start.36 = (bf16[2,9,32,128]{3,2,1,0:T(8,128)(2,1)S(1)}, bf16[2,9,32,128]{3,2,1,0:T(8,128)(2,1)S(1)}, u32[]{:S(2)}, u32[]{:S(2)}) collective-permute-start(bf16[2,9,32,128]{3,2,1,0:T(8,128)(2,1)S(1)} %pad_maximum_fusion.1.refs_0_), channel_id=1, source_target_pairs={{0,12},{1,11},{2,14},{3,9},{4,8},{5,15},{6,10},{7,13},{8,4},{9,3},... | collective-permute-start | bytes 442376 | tf_op jit(solution)/shard_map/ppermute | solution.py:224
  108.2 0.9 copy-done.15
  109.1 0.6 shard_map.104.near_ref
  109.8 1.5 collective-permute-done.36.refs_6_
  111.3 3.8 %collective-permute-done.37.refs_7_ = bf16[2,9,32,128]{3,2,1,0:T(8,128)(2,1)S(1)} collective-permute-done((bf16[2,9,32,128]{3,2,1,0:T(8,128)(2,1)S(1)}, bf16[2,9,32,128]{3,2,1,0:T(8,128)(2,1)S(1)}, u32[]{:S(2)}, u32[]{:S(2)}) %collective-permute-start.37) | collective-permute-done | bytes 147488 | tf_op jit(solution)/shard_map/ppermute | solution.py:224
  118.1 5.3 %shard_map.106 = (bf16[4,2,9,32,128]{4,3,2,1,0:T(8,128)(2,1)S(1)}, bf16[4,2,9,32,128]{4,3,2,1,0:T(8,128)(2,1)S(1)}, bf16[4,2,9,32,128]{4,3,2,1,0:T(8,128)(2,1)S(1)}, bf16[4,2,9,32,128]{4,3,2,1,0:T(8,128)(2,1)S(1)}) custom-call(s32[128]{0:T(128)S(1)} %get-tuple-element.120.source_ref, s32[128]{0:T(128)S(1)} %get-tuple-element.121.target_ref, ...), custom_call_target="tpu_custom_call" | custom-call | flops 75497472 | bytes 10485760 | tf_op jit(solution)/shard_map/pallas_call | solution.py:348
  124.0 1.5 collective-permute-done.49.swap_ref
  125.7 1.6 %collective-permute-start.50 = (bf16[2,9,32,128]{3,2,1,0:T(8,128)(2,1)S(1)}, bf16[2,9,32,128]{3,2,1,0:T(8,128)(2,1)S(1)}, u32[]{:S(2)}, u32[]{:S(2)}) collective-permute-start(bf16[2,9,32,128]{3,2,1,0:T(8,128)(2,1)S(1)} %get-tuple-element.111), channel_id=1, source_target_pairs={{0,14},{1,15},{2,12},{3,13},{4,10},{5,11},{6,8},{7,9},{8,6},{9,7},... | collective-permute-start | bytes 442376 | tf_op jit(solution)/shard_map/ppermute | solution.py:224
  127.3 1.1 collective-permute-start.51
  128.8 2.9 %collective-permute-start.53 = (bf16[2,9,32,128]{3,2,1,0:T(8,128)(2,1)S(1)}, bf16[2,9,32,128]{3,2,1,0:T(8,128)(2,1)S(1)}, u32[]{:S(2)}, u32[]{:S(2)}) collective-permute-start(bf16[2,9,32,128]{3,2,1,0:T(8,128)(2,1)S(1)} %get-tuple-element.114), channel_id=1, source_target_pairs={{0,10},{1,7},{2,8},{3,5},{4,14},{5,3},{6,12},{7,1},{8,2},{9,15},{1... | collective-permute-start | bytes 442376 | tf_op jit(solution)/shard_map/ppermute | solution.py:224
  131.8 0.6 collective-permute-start.54
  132.5 3.3 %collective-permute-done.50.refs_0_ = bf16[2,9,32,128]{3,2,1,0:T(8,128)(2,1)S(1)} collective-permute-done((bf16[2,9,32,128]{3,2,1,0:T(8,128)(2,1)S(1)}, bf16[2,9,32,128]{3,2,1,0:T(8,128)(2,1)S(1)}, u32[]{:S(2)}, u32[]{:S(2)}) %collective-permute-start.50) | collective-permute-done | bytes 147488 | tf_op jit(solution)/shard_map/ppermute | solution.py:224
  135.8 6.7 %collective-permute-done.51.refs_1_ = bf16[2,9,32,128]{3,2,1,0:T(8,128)(2,1)S(1)} collective-permute-done((bf16[2,9,32,128]{3,2,1,0:T(8,128)(2,1)S(1)}, bf16[2,9,32,128]{3,2,1,0:T(8,128)(2,1)S(1)}, u32[]{:S(2)}, u32[]{:S(2)}) %collective-permute-start.51) | collective-permute-done | bytes 147488 | tf_op jit(solution)/shard_map/ppermute | solution.py:224
  142.5 0.7 collective-permute-done.54.refs_4_
  143.2 4.8 %collective-permute-done.56.refs_6_ = bf16[2,9,32,128]{3,2,1,0:T(8,128)(2,1)S(1)} collective-permute-done((bf16[2,9,32,128]{3,2,1,0:T(8,128)(2,1)S(1)}, bf16[2,9,32,128]{3,2,1,0:T(8,128)(2,1)S(1)}, u32[]{:S(2)}, u32[]{:S(2)}) %collective-permute-start.56) | collective-permute-done | bytes 147488 | tf_op jit(solution)/shard_map/ppermute | solution.py:224
  148.8 0.7 collective-permute-done.38.inner_ref
  149.8 4.4 %collective-permute-done.57.rest_0_ = bf16[9,32,128]{2,1,0:T(8,128)(2,1)S(1)} collective-permute-done((bf16[9,32,128]{2,1,0:T(8,128)(2,1)S(1)}, bf16[9,32,128]{2,1,0:T(8,128)(2,1)S(1)}, u32[]{:S(2)}, u32[]{:S(2)}) %collective-permute-start.57) | collective-permute-done | bytes 73760 | tf_op jit(solution)/shard_map/ppermute | solution.py:220
  154.1 2.5 %shard_map.110 = bf16[8,32,256]{2,1,0:T(8,128)(2,1)} custom-call(s32[12]{0:T(128)S(1)} %copy-done.16, s32[1]{0:T(128)} %bitcast.core_ref, f32[8,32,256]{2,1,0:T(8,128)S(1)} %shard_map.104.near_ref, f32[2,32,256]{2,1,0:T(8,128)S(1)} %shard_map.105.edge_ref, bf16[8,96,256]{2,1,0:T(8,128)(2,1)S(1)} %copy-done.2, bf16[8,96,96]{2,1,0:T(8,128)(2,1)S(1)} %copy-done.3, ...), custom_call_target="tpu_custom_call" | custom-call | tf_op jit(solution)/shard_map/pallas_call | solution.py:362
  (114 shorter events, 10.2 us)
Async XLA Ops:
  3.5 10.2 %collective-permute-start = (bf16[9,32,128]{2,1,0:T(8,128)(2,1)}, bf16[9,32,128]{2,1,0:T(8,128)(2,1)S(1)}, u32[]{:S(2)}, u32[]{:S(2)}) collective-permute-start(bf16[9,32,128]{2,1,0:T(8,128)(2,1)} %get-tuple-element.62), channel_id=1, source_target_pairs={{0,16},{1,17},{2,18},{3,19},{4,20},{5,21},{6,22},{7,23},{8,24},{9,... | collective-permute-start | bytes 221192 | tf_op jit(solution)/shard_map/ppermute | solution.py:220
  7.6 6.1 %collective-permute-start.1 = (bf16[1,32,256]{2,1,0:T(8,128)(2,1)}, bf16[1,32,256]{2,1,0:T(8,128)(2,1)S(1)}, u32[]{:S(2)}, u32[]{:S(2)}) collective-permute-start(bf16[1,32,256]{2,1,0:T(8,128)(2,1)} %get-tuple-element.63), channel_id=1, source_target_pairs={{1,3},{3,5},{5,7},{7,9},{9,11},{11,13},{13,15},{15,17},{17,19},{19... | collective-permute-start | bytes 49160 | tf_op jit(solution)/shard_map/ppermute | solution.py:340
  13.7 14.4 %copy-start = (bf16[8,3,256,256]{3,2,1,0:T(8,128)(2,1)S(1)}, bf16[8,3,256,256]{3,2,1,0:T(8,128)(2,1)}, u32[]{:S(2)}) copy-start(bf16[8,3,256,256]{3,2,1,0:T(8,128)(2,1)} %last_ref.3) | copy-start | bytes 9437188
  13.7 11.7 %copy-start.19 = (bf16[1,32,256]{2,1,0:T(8,128)(2,1)}, bf16[1,32,256]{2,1,0:T(8,128)(2,1)S(1)}, u32[]{:S(2)}) copy-start(bf16[1,32,256]{2,1,0:T(8,128)(2,1)S(1)} %collective-permute-done.1) | copy-start | bytes 49156
  14.6 8.1 %collective-permute-start.2 = (bf16[2,9,32,128]{3,2,1,0:T(8,128)(2,1)S(1)}, bf16[2,9,32,128]{3,2,1,0:T(8,128)(2,1)}, u32[]{:S(2)}, u32[]{:S(2)}) collective-permute-start(bf16[2,9,32,128]{3,2,1,0:T(8,128)(2,1)S(1)} %pad_maximum_fusion.refs_0_), channel_id=1, source_target_pairs={{0,2},{1,5},{2,0},{3,7},{4,6},{5,1},{6,4},{7,3},{8,10},{9,13},{10,... | collective-permute-start | bytes 442376 | tf_op jit(solution)/shard_map/ppermute | solution.py:224
  17.3 8.1 %collective-permute-start.3 = (bf16[2,9,32,128]{3,2,1,0:T(8,128)(2,1)S(1)}, bf16[2,9,32,128]{3,2,1,0:T(8,128)(2,1)}, u32[]{:S(2)}, u32[]{:S(2)}) collective-permute-start(bf16[2,9,32,128]{3,2,1,0:T(8,128)(2,1)S(1)} %pad_maximum_fusion.refs_0_), channel_id=1, source_target_pairs={{0,4},{1,9},{2,6},{3,11},{4,0},{5,13},{6,2},{7,15},{8,12},{9,1},{1... | collective-permute-start | bytes 442376 | tf_op jit(solution)/shard_map/ppermute | solution.py:224
  18.8 12.6 %collective-permute-start.4 = (bf16[2,9,32,128]{3,2,1,0:T(8,128)(2,1)S(1)}, bf16[2,9,32,128]{3,2,1,0:T(8,128)(2,1)S(1)}, u32[]{:S(2)}, u32[]{:S(2)}) collective-permute-start(bf16[2,9,32,128]{3,2,1,0:T(8,128)(2,1)S(1)} %pad_maximum_fusion.refs_0_), channel_id=1, source_target_pairs={{0,6},{1,13},{2,4},{3,15},{4,2},{5,9},{6,0},{7,11},{8,14},{9,5},{1... | collective-permute-start | bytes 442376 | tf_op jit(solution)/shard_map/ppermute | solution.py:224
  19.7 11.8 %collective-permute-start.5 = (bf16[2,9,32,128]{3,2,1,0:T(8,128)(2,1)S(1)}, bf16[2,9,32,128]{3,2,1,0:T(8,128)(2,1)S(1)}, u32[]{:S(2)}, u32[]{:S(2)}) collective-permute-start(bf16[2,9,32,128]{3,2,1,0:T(8,128)(2,1)S(1)} %pad_maximum_fusion.refs_0_), channel_id=1, source_target_pairs={{0,8},{1,3},{2,10},{3,1},{4,12},{5,7},{6,14},{7,5},{8,0},{9,11},{1... | collective-permute-start | bytes 442376 | tf_op jit(solution)/shard_map/ppermute | solution.py:224
  22.7 8.8 %collective-permute-start.6 = (bf16[2,9,32,128]{3,2,1,0:T(8,128)(2,1)S(1)}, bf16[2,9,32,128]{3,2,1,0:T(8,128)(2,1)S(1)}, u32[]{:S(2)}, u32[]{:S(2)}) collective-permute-start(bf16[2,9,32,128]{3,2,1,0:T(8,128)(2,1)S(1)} %pad_maximum_fusion.refs_0_), channel_id=1, source_target_pairs={{0,10},{1,7},{2,8},{3,5},{4,14},{5,3},{6,12},{7,1},{8,2},{9,15},{1... | collective-permute-start | bytes 442376 | tf_op jit(solution)/shard_map/ppermute | solution.py:224
  22.7 11.6 %collective-permute-start.7 = (bf16[2,9,32,128]{3,2,1,0:T(8,128)(2,1)S(1)}, bf16[2,9,32,128]{3,2,1,0:T(8,128)(2,1)S(1)}, u32[]{:S(2)}, u32[]{:S(2)}) collective-permute-start(bf16[2,9,32,128]{3,2,1,0:T(8,128)(2,1)S(1)} %pad_maximum_fusion.refs_0_), channel_id=1, source_target_pairs={{0,12},{1,11},{2,14},{3,9},{4,8},{5,15},{6,10},{7,13},{8,4},{9,3},... | collective-permute-start | bytes 442376 | tf_op jit(solution)/shard_map/ppermute | solution.py:224
  25.4 10.0 %collective-permute-start.8 = (bf16[2,9,32,128]{3,2,1,0:T(8,128)(2,1)S(1)}, bf16[2,9,32,128]{3,2,1,0:T(8,128)(2,1)S(1)}, u32[]{:S(2)}, u32[]{:S(2)}) collective-permute-start(bf16[2,9,32,128]{3,2,1,0:T(8,128)(2,1)S(1)} %pad_maximum_fusion.refs_0_), channel_id=1, source_target_pairs={{0,14},{1,15},{2,12},{3,13},{4,10},{5,11},{6,8},{7,9},{8,6},{9,7},... | collective-permute-start | bytes 442376 | tf_op jit(solution)/shard_map/ppermute | solution.py:224
  31.5 4.0 %copy-start.5 = (bf16[2,9,32,128]{3,2,1,0:T(8,128)(2,1)}, bf16[2,9,32,128]{3,2,1,0:T(8,128)(2,1)S(1)}, u32[]{:S(2)}) copy-start(bf16[2,9,32,128]{3,2,1,0:T(8,128)(2,1)S(1)} %collective-permute-done.4.refs_3_) | copy-start | bytes 442372
  31.5 5.2 %collective-permute-start.11 = (bf16[2,9,32,128]{3,2,1,0:T(8,128)(2,1)S(1)}, bf16[2,9,32,128]{3,2,1,0:T(8,128)(2,1)}, u32[]{:S(2)}, u32[]{:S(2)}) collective-permute-start(bf16[2,9,32,128]{3,2,1,0:T(8,128)(2,1)S(1)} %pad_maximum_fusion.refs_0_), channel_id=1, source_target_pairs={{0,1},{1,0},{2,3},{3,2},{4,5},{5,4},{6,7},{7,6},{8,9},{9,8},{10,11... | collective-permute-start | bytes 442376 | tf_op jit(solution)/shard_map/ppermute | solution.py:229
  31.5 4.0 %copy-start.7 = (bf16[2,9,32,128]{3,2,1,0:T(8,128)(2,1)}, bf16[2,9,32,128]{3,2,1,0:T(8,128)(2,1)S(1)}, u32[]{:S(2)}) copy-start(bf16[2,9,32,128]{3,2,1,0:T(8,128)(2,1)S(1)} %collective-permute-done.5.refs_4_) | copy-start | bytes 442372
  35.5 1.7 %collective-permute-start.12 = (bf16[2,9,32,128]{3,2,1,0:T(8,128)(2,1)}, bf16[2,9,32,128]{3,2,1,0:T(8,128)(2,1)}, u32[]{:S(2)}, u32[]{:S(2)}) collective-permute-start(bf16[2,9,32,128]{3,2,1,0:T(8,128)(2,1)} %collective-permute-done.2.refs_1_), channel_id=1, source_target_pairs={{0,1},{1,0},{2,3},{3,2},{4,5},{5,4},{6,7},{7,6},{8,9},{9,8},{10,11... | collective-permute-start | bytes 442376 | tf_op jit(solution)/shard_map/ppermute | solution.py:229
  36.1 1.9 %collective-permute-start.13 = (bf16[2,9,32,128]{3,2,1,0:T(8,128)(2,1)}, bf16[2,9,32,128]{3,2,1,0:T(8,128)(2,1)}, u32[]{:S(2)}, u32[]{:S(2)}) collective-permute-start(bf16[2,9,32,128]{3,2,1,0:T(8,128)(2,1)} %collective-permute-done.3.refs_2_), channel_id=1, source_target_pairs={{0,1},{1,0},{2,3},{3,2},{4,5},{5,4},{6,7},{7,6},{8,9},{9,8},{10,11... | collective-permute-start | bytes 442376 | tf_op jit(solution)/shard_map/ppermute | solution.py:229
  36.1 2.7 %collective-permute-start.14 = (bf16[2,9,32,128]{3,2,1,0:T(8,128)(2,1)}, bf16[2,9,32,128]{3,2,1,0:T(8,128)(2,1)S(1)}, u32[]{:S(2)}, u32[]{:S(2)}) collective-permute-start(bf16[2,9,32,128]{3,2,1,0:T(8,128)(2,1)} %copy-done.5), channel_id=1, source_target_pairs={{0,1},{1,0},{2,3},{3,2},{4,5},{5,4},{6,7},{7,6},{8,9},{9,8},{10,11... | collective-permute-start | bytes 442376 | tf_op jit(solution)/shard_map/ppermute | solution.py:229
  36.7 2.2 %collective-permute-start.15 = (bf16[2,9,32,128]{3,2,1,0:T(8,128)(2,1)}, bf16[2,9,32,128]{3,2,1,0:T(8,128)(2,1)S(1)}, u32[]{:S(2)}, u32[]{:S(2)}) collective-permute-start(bf16[2,9,32,128]{3,2,1,0:T(8,128)(2,1)} %copy-done.7), channel_id=1, source_target_pairs={{0,1},{1,0},{2,3},{3,2},{4,5},{5,4},{6,7},{7,6},{8,9},{9,8},{10,11... | collective-permute-start | bytes 442376 | tf_op jit(solution)/shard_map/ppermute | solution.py:229
  36.7 2.3 %collective-permute-start.16 = (bf16[2,9,32,128]{3,2,1,0:T(8,128)(2,1)}, bf16[2,9,32,128]{3,2,1,0:T(8,128)(2,1)S(1)}, u32[]{:S(2)}, u32[]{:S(2)}) collective-permute-start(bf16[2,9,32,128]{3,2,1,0:T(8,128)(2,1)} %copy-done.9), channel_id=1, source_target_pairs={{0,1},{1,0},{2,3},{3,2},{4,5},{5,4},{6,7},{7,6},{8,9},{9,8},{10,11... | collective-permute-start | bytes 442376 | tf_op jit(solution)/shard_map/ppermute | solution.py:229
  37.2 1.7 %collective-permute-start.17 = (bf16[2,9,32,128]{3,2,1,0:T(8,128)(2,1)}, bf16[2,9,32,128]{3,2,1,0:T(8,128)(2,1)S(1)}, u32[]{:S(2)}, u32[]{:S(2)}) collective-permute-start(bf16[2,9,32,128]{3,2,1,0:T(8,128)(2,1)} %copy-done.11), channel_id=1, source_target_pairs={{0,1},{1,0},{2,3},{3,2},{4,5},{5,4},{6,7},{7,6},{8,9},{9,8},{10,11... | collective-permute-start | bytes 442376 | tf_op jit(solution)/shard_map/ppermute | solution.py:229
  38.0 1.6 %collective-permute-start.18 = (bf16[2,9,32,128]{3,2,1,0:T(8,128)(2,1)}, bf16[2,9,32,128]{3,2,1,0:T(8,128)(2,1)S(1)}, u32[]{:S(2)}, u32[]{:S(2)}) collective-permute-start(bf16[2,9,32,128]{3,2,1,0:T(8,128)(2,1)} %copy-done.13), channel_id=1, source_target_pairs={{0,1},{1,0},{2,3},{3,2},{4,5},{5,4},{6,7},{7,6},{8,9},{9,8},{10,11... | collective-permute-start | bytes 442376 | tf_op jit(solution)/shard_map/ppermute | solution.py:229
  52.1 26.5 %copy-start.18 = (bf16[1,32,256]{2,1,0:T(8,128)(2,1)S(1)}, bf16[1,32,256]{2,1,0:T(8,128)(2,1)}, u32[]{:S(2)}) copy-start(bf16[1,32,256]{2,1,0:T(8,128)(2,1)} %get-tuple-element.67) | copy-start | bytes 49156
  52.1 26.6 %copy-start.20 = (bf16[1,32,256]{2,1,0:T(8,128)(2,1)S(1)}, bf16[1,32,256]{2,1,0:T(8,128)(2,1)}, u32[]{:S(2)}) copy-start(bf16[1,32,256]{2,1,0:T(8,128)(2,1)} %copy-done.19) | copy-start | bytes 49156
  52.1 2.1 %collective-permute-start.20 = (bf16[4,2,9,32,128]{4,3,2,1,0:T(8,128)(2,1)S(1)}, bf16[4,2,9,32,128]{4,3,2,1,0:T(8,128)(2,1)S(1)}, u32[]{:S(2)}, u32[]{:S(2)}) collective-permute-start(bf16[4,2,9,32,128]{4,3,2,1,0:T(8,128)(2,1)S(1)} %get-tuple-element.81), channel_id=1, source_target_pairs={{0,1},{1,0},{2,3},{3,2},{4,5},{5,4},{6,7},{7,6},{8,9},{9,8},{10,11... | collective-permute-start | bytes 1769480 | tf_op jit(solution)/shard_map/ppermute | solution.py:229
  52.3 8.4 %collective-permute-start.19 = (bf16[4,2,9,32,128]{4,3,2,1,0:T(8,128)(2,1)S(1)}, bf16[4,2,9,32,128]{4,3,2,1,0:T(8,128)(2,1)S(1)}, u32[]{:S(2)}, u32[]{:S(2)}) collective-permute-start(bf16[4,2,9,32,128]{4,3,2,1,0:T(8,128)(2,1)S(1)} %get-tuple-element.78), channel_id=1, source_target_pairs={{0,1},{1,0},{2,3},{3,2},{4,5},{5,4},{6,7},{7,6},{8,9},{9,8},{10,11... | collective-permute-start | bytes 1769480 | tf_op jit(solution)/shard_map/ppermute | solution.py:229
  54.3 9.4 %collective-permute-start.21 = (bf16[2,9,32,128]{3,2,1,0:T(8,128)(2,1)S(1)}, bf16[2,9,32,128]{3,2,1,0:T(8,128)(2,1)S(1)}, u32[]{:S(2)}, u32[]{:S(2)}) collective-permute-start(bf16[2,9,32,128]{3,2,1,0:T(8,128)(2,1)S(1)} %get-tuple-element.82), channel_id=1, source_target_pairs={{0,14},{1,15},{2,12},{3,13},{4,10},{5,11},{6,8},{7,9},{8,6},{9,7},... | collective-permute-start | bytes 442376 | tf_op jit(solution)/shard_map/ppermute | solution.py:224
  56.3 13.0 %collective-permute-start.22 = (bf16[2,9,32,128]{3,2,1,0:T(8,128)(2,1)S(1)}, bf16[2,9,32,128]{3,2,1,0:T(8,128)(2,1)S(1)}, u32[]{:S(2)}, u32[]{:S(2)}) collective-permute-start(bf16[2,9,32,128]{3,2,1,0:T(8,128)(2,1)S(1)} %get-tuple-element.83), channel_id=1, source_target_pairs={{0,6},{1,13},{2,4},{3,15},{4,2},{5,9},{6,0},{7,11},{8,14},{9,5},{1... | collective-permute-start | bytes 442376 | tf_op jit(solution)/shard_map/ppermute | solution.py:224
  58.3 13.1 %collective-permute-start.23 = (bf16[2,9,32,128]{3,2,1,0:T(8,128)(2,1)S(1)}, bf16[2,9,32,128]{3,2,1,0:T(8,128)(2,1)S(1)}, u32[]{:S(2)}, u32[]{:S(2)}) collective-permute-start(bf16[2,9,32,128]{3,2,1,0:T(8,128)(2,1)S(1)} %get-tuple-element.84), channel_id=1, source_target_pairs={{0,12},{1,11},{2,14},{3,9},{4,8},{5,15},{6,10},{7,13},{8,4},{9,3},... | collective-permute-start | bytes 442376 | tf_op jit(solution)/shard_map/ppermute | solution.py:224
  58.3 13.1 %collective-permute-start.24 = (bf16[2,9,32,128]{3,2,1,0:T(8,128)(2,1)S(1)}, bf16[2,9,32,128]{3,2,1,0:T(8,128)(2,1)S(1)}, u32[]{:S(2)}, u32[]{:S(2)}) collective-permute-start(bf16[2,9,32,128]{3,2,1,0:T(8,128)(2,1)S(1)} %get-tuple-element.85), channel_id=1, source_target_pairs={{0,10},{1,7},{2,8},{3,5},{4,14},{5,3},{6,12},{7,1},{8,2},{9,15},{1... | collective-permute-start | bytes 442376 | tf_op jit(solution)/shard_map/ppermute | solution.py:224
  60.8 10.6 %collective-permute-start.25 = (bf16[2,9,32,128]{3,2,1,0:T(8,128)(2,1)S(1)}, bf16[2,9,32,128]{3,2,1,0:T(8,128)(2,1)S(1)}, u32[]{:S(2)}, u32[]{:S(2)}) collective-permute-start(bf16[2,9,32,128]{3,2,1,0:T(8,128)(2,1)S(1)} %get-tuple-element.86), channel_id=1, source_target_pairs={{0,2},{1,5},{2,0},{3,7},{4,6},{5,1},{6,4},{7,3},{8,10},{9,13},{10,... | collective-permute-start | bytes 442376 | tf_op jit(solution)/shard_map/ppermute | solution.py:224
  63.7 7.9 %collective-permute-start.26 = (bf16[2,9,32,128]{3,2,1,0:T(8,128)(2,1)S(1)}, bf16[2,9,32,128]{3,2,1,0:T(8,128)(2,1)S(1)}, u32[]{:S(2)}, u32[]{:S(2)}) collective-permute-start(bf16[2,9,32,128]{3,2,1,0:T(8,128)(2,1)S(1)} %get-tuple-element.87), channel_id=1, source_target_pairs={{0,4},{1,9},{2,6},{3,11},{4,0},{5,13},{6,2},{7,15},{8,12},{9,1},{1... | collective-permute-start | bytes 442376 | tf_op jit(solution)/shard_map/ppermute | solution.py:224
  69.3 5.2 %collective-permute-start.27 = (bf16[2,9,32,128]{3,2,1,0:T(8,128)(2,1)S(1)}, bf16[2,9,32,128]{3,2,1,0:T(8,128)(2,1)S(1)}, u32[]{:S(2)}, u32[]{:S(2)}) collective-permute-start(bf16[2,9,32,128]{3,2,1,0:T(8,128)(2,1)S(1)} %get-tuple-element.88), channel_id=1, source_target_pairs={{0,8},{1,3},{2,10},{3,1},{4,12},{5,7},{6,14},{7,5},{8,0},{9,11},{1... | collective-permute-start | bytes 442376 | tf_op jit(solution)/shard_map/ppermute | solution.py:224
  74.7 7.6 %collective-permute-start.28 = (bf16[9,32,128]{2,1,0:T(8,128)(2,1)S(1)}, bf16[9,32,128]{2,1,0:T(8,128)(2,1)S(1)}, u32[]{:S(2)}, u32[]{:S(2)}) collective-permute-start(bf16[9,32,128]{2,1,0:T(8,128)(2,1)S(1)} %get-tuple-element.90), channel_id=1, source_target_pairs={{0,16},{1,17},{2,18},{3,19},{4,20},{5,21},{6,22},{7,23},{8,24},{9,... | collective-permute-start | bytes 221192 | tf_op jit(solution)/shard_map/ppermute | solution.py:220
  78.6 1.2 collective-permute-start.9
  78.6 1.3 collective-permute-start.10
  84.8 8.4 %collective-permute-start.29 = (bf16[9,32,128]{2,1,0:T(8,128)(2,1)S(1)}, bf16[9,32,128]{2,1,0:T(8,128)(2,1)S(1)}, u32[]{:S(2)}, u32[]{:S(2)}) collective-permute-start(bf16[9,32,128]{2,1,0:T(8,128)(2,1)S(1)} %get-tuple-element.92), channel_id=1, source_target_pairs={{0,16},{1,17},{2,18},{3,19},{4,20},{5,21},{6,22},{7,23},{8,24},{9,... | collective-permute-start | bytes 221192 | tf_op jit(solution)/shard_map/ppermute | solution.py:220
  86.4 6.8 %collective-permute-start.30 = (bf16[1,32,256]{2,1,0:T(8,128)(2,1)S(1)}, bf16[1,32,256]{2,1,0:T(8,128)(2,1)S(1)}, u32[]{:S(2)}, u32[]{:S(2)}) collective-permute-start(bf16[1,32,256]{2,1,0:T(8,128)(2,1)S(1)} %get-tuple-element.93), channel_id=1, source_target_pairs={{1,3},{3,5},{5,7},{7,9},{9,11},{11,13},{13,15},{15,17},{17,19},{19... | collective-permute-start | bytes 49160 | tf_op jit(solution)/shard_map/ppermute | solution.py:340
  93.2 10.8 %collective-permute-start.31 = (bf16[2,9,32,128]{3,2,1,0:T(8,128)(2,1)S(1)}, bf16[2,9,32,128]{3,2,1,0:T(8,128)(2,1)S(1)}, u32[]{:S(2)}, u32[]{:S(2)}) collective-permute-start(bf16[2,9,32,128]{3,2,1,0:T(8,128)(2,1)S(1)} %pad_maximum_fusion.1.refs_0_), channel_id=1, source_target_pairs={{0,2},{1,5},{2,0},{3,7},{4,6},{5,1},{6,4},{7,3},{8,10},{9,13},{10,... | collective-permute-start | bytes 442376 | tf_op jit(solution)/shard_map/ppermute | solution.py:224
  96.2 12.0 %collective-permute-start.32 = (bf16[2,9,32,128]{3,2,1,0:T(8,128)(2,1)S(1)}, bf16[2,9,32,128]{3,2,1,0:T(8,128)(2,1)S(1)}, u32[]{:S(2)}, u32[]{:S(2)}) collective-permute-start(bf16[2,9,32,128]{3,2,1,0:T(8,128)(2,1)S(1)} %pad_maximum_fusion.1.refs_0_), channel_id=1, source_target_pairs={{0,4},{1,9},{2,6},{3,11},{4,0},{5,13},{6,2},{7,15},{8,12},{9,1},{1... | collective-permute-start | bytes 442376 | tf_op jit(solution)/shard_map/ppermute | solution.py:224
  96.2 13.5 %collective-permute-start.33 = (bf16[2,9,32,128]{3,2,1,0:T(8,128)(2,1)S(1)}, bf16[2,9,32,128]{3,2,1,0:T(8,128)(2,1)S(1)}, u32[]{:S(2)}, u32[]{:S(2)}) collective-permute-start(bf16[2,9,32,128]{3,2,1,0:T(8,128)(2,1)S(1)} %pad_maximum_fusion.1.refs_0_), channel_id=1, source_target_pairs={{0,6},{1,13},{2,4},{3,15},{4,2},{5,9},{6,0},{7,11},{8,14},{9,5},{1... | collective-permute-start | bytes 442376 | tf_op jit(solution)/shard_map/ppermute | solution.py:224
  97.7 12.1 %collective-permute-start.34 = (bf16[2,9,32,128]{3,2,1,0:T(8,128)(2,1)S(1)}, bf16[2,9,32,128]{3,2,1,0:T(8,128)(2,1)S(1)}, u32[]{:S(2)}, u32[]{:S(2)}) collective-permute-start(bf16[2,9,32,128]{3,2,1,0:T(8,128)(2,1)S(1)} %pad_maximum_fusion.1.refs_0_), channel_id=1, source_target_pairs={{0,8},{1,3},{2,10},{3,1},{4,12},{5,7},{6,14},{7,5},{8,0},{9,11},{1... | collective-permute-start | bytes 442376 | tf_op jit(solution)/shard_map/ppermute | solution.py:224
  99.0 10.8 %collective-permute-start.35 = (bf16[2,9,32,128]{3,2,1,0:T(8,128)(2,1)S(1)}, bf16[2,9,32,128]{3,2,1,0:T(8,128)(2,1)S(1)}, u32[]{:S(2)}, u32[]{:S(2)}) collective-permute-start(bf16[2,9,32,128]{3,2,1,0:T(8,128)(2,1)S(1)} %pad_maximum_fusion.1.refs_0_), channel_id=1, source_target_pairs={{0,10},{1,7},{2,8},{3,5},{4,14},{5,3},{6,12},{7,1},{8,2},{9,15},{1... | collective-permute-start | bytes 442376 | tf_op jit(solution)/shard_map/ppermute | solution.py:224
  104.0 7.3 %collective-permute-start.36 = (bf16[2,9,32,128]{3,2,1,0:T(8,128)(2,1)S(1)}, bf16[2,9,32,128]{3,2,1,0:T(8,128)(2,1)S(1)}, u32[]{:S(2)}, u32[]{:S(2)}) collective-permute-start(bf16[2,9,32,128]{3,2,1,0:T(8,128)(2,1)S(1)} %pad_maximum_fusion.1.refs_0_), channel_id=1, source_target_pairs={{0,12},{1,11},{2,14},{3,9},{4,8},{5,15},{6,10},{7,13},{8,4},{9,3},... | collective-permute-start | bytes 442376 | tf_op jit(solution)/shard_map/ppermute | solution.py:224
  108.2 6.9 %collective-permute-start.37 = (bf16[2,9,32,128]{3,2,1,0:T(8,128)(2,1)S(1)}, bf16[2,9,32,128]{3,2,1,0:T(8,128)(2,1)S(1)}, u32[]{:S(2)}, u32[]{:S(2)}) collective-permute-start(bf16[2,9,32,128]{3,2,1,0:T(8,128)(2,1)S(1)} %pad_maximum_fusion.1.refs_0_), channel_id=1, source_target_pairs={{0,14},{1,15},{2,12},{3,13},{4,10},{5,11},{6,8},{7,9},{8,6},{9,7},... | collective-permute-start | bytes 442376 | tf_op jit(solution)/shard_map/ppermute | solution.py:224
  109.7 6.5 %collective-permute-start.40 = (bf16[2,9,32,128]{3,2,1,0:T(8,128)(2,1)S(1)}, bf16[2,9,32,128]{3,2,1,0:T(8,128)(2,1)S(1)}, u32[]{:S(2)}, u32[]{:S(2)}) collective-permute-start(bf16[2,9,32,128]{3,2,1,0:T(8,128)(2,1)S(1)} %pad_maximum_fusion.1.refs_0_), channel_id=1, source_target_pairs={{0,1},{1,0},{2,3},{3,2},{4,5},{5,4},{6,7},{7,6},{8,9},{9,8},{10,11... | collective-permute-start | bytes 442376 | tf_op jit(solution)/shard_map/ppermute | solution.py:229
  115.2 1.4 collective-permute-start.41
  115.2 1.6 %collective-permute-start.42 = (bf16[2,9,32,128]{3,2,1,0:T(8,128)(2,1)S(1)}, bf16[2,9,32,128]{3,2,1,0:T(8,128)(2,1)S(1)}, u32[]{:S(2)}, u32[]{:S(2)}) collective-permute-start(bf16[2,9,32,128]{3,2,1,0:T(8,128)(2,1)S(1)} %collective-permute-done.32.refs_2_), channel_id=1, source_target_pairs={{0,1},{1,0},{2,3},{3,2},{4,5},{5,4},{6,7},{7,6},{8,9},{9,8},{10,11... | collective-permute-start | bytes 442376 | tf_op jit(solution)/shard_map/ppermute | solution.py:229
  115.7 1.4 collective-permute-start.43
  115.7 1.6 %collective-permute-start.44 = (bf16[2,9,32,128]{3,2,1,0:T(8,128)(2,1)S(1)}, bf16[2,9,32,128]{3,2,1,0:T(8,128)(2,1)S(1)}, u32[]{:S(2)}, u32[]{:S(2)}) collective-permute-start(bf16[2,9,32,128]{3,2,1,0:T(8,128)(2,1)S(1)} %collective-permute-done.34.refs_4_), channel_id=1, source_target_pairs={{0,1},{1,0},{2,3},{3,2},{4,5},{5,4},{6,7},{7,6},{8,9},{9,8},{10,11... | collective-permute-start | bytes 442376 | tf_op jit(solution)/shard_map/ppermute | solution.py:229
  116.2 1.4 collective-permute-start.45
  116.5 1.4 collective-permute-start.46
  116.7 1.4 collective-permute-start.47
  123.5 2.1 %collective-permute-start.49 = (bf16[4,2,9,32,128]{4,3,2,1,0:T(8,128)(2,1)S(1)}, bf16[4,2,9,32,128]{4,3,2,1,0:T(8,128)(2,1)S(1)}, u32[]{:S(2)}, u32[]{:S(2)}) collective-permute-start(bf16[4,2,9,32,128]{4,3,2,1,0:T(8,128)(2,1)S(1)} %get-tuple-element.110), channel_id=1, source_target_pairs={{0,1},{1,0},{2,3},{3,2},{4,5},{5,4},{6,7},{7,6},{8,9},{9,8},{10,11... | collective-permute-start | bytes 1769480 | tf_op jit(solution)/shard_map/ppermute | solution.py:229
  123.8 7.9 %collective-permute-start.48 = (bf16[4,2,9,32,128]{4,3,2,1,0:T(8,128)(2,1)S(1)}, bf16[4,2,9,32,128]{4,3,2,1,0:T(8,128)(2,1)S(1)}, u32[]{:S(2)}, u32[]{:S(2)}) collective-permute-start(bf16[4,2,9,32,128]{4,3,2,1,0:T(8,128)(2,1)S(1)} %get-tuple-element.107), channel_id=1, source_target_pairs={{0,1},{1,0},{2,3},{3,2},{4,5},{5,4},{6,7},{7,6},{8,9},{9,8},{10,11... | collective-permute-start | bytes 1769480 | tf_op jit(solution)/shard_map/ppermute | solution.py:229
  125.7 10.1 %collective-permute-start.50 = (bf16[2,9,32,128]{3,2,1,0:T(8,128)(2,1)S(1)}, bf16[2,9,32,128]{3,2,1,0:T(8,128)(2,1)S(1)}, u32[]{:S(2)}, u32[]{:S(2)}) collective-permute-start(bf16[2,9,32,128]{3,2,1,0:T(8,128)(2,1)S(1)} %get-tuple-element.111), channel_id=1, source_target_pairs={{0,14},{1,15},{2,12},{3,13},{4,10},{5,11},{6,8},{7,9},{8,6},{9,7},... | collective-permute-start | bytes 442376 | tf_op jit(solution)/shard_map/ppermute | solution.py:224
  127.3 15.2 %collective-permute-start.51 = (bf16[2,9,32,128]{3,2,1,0:T(8,128)(2,1)S(1)}, bf16[2,9,32,128]{3,2,1,0:T(8,128)(2,1)S(1)}, u32[]{:S(2)}, u32[]{:S(2)}) collective-permute-start(bf16[2,9,32,128]{3,2,1,0:T(8,128)(2,1)S(1)} %get-tuple-element.112), channel_id=1, source_target_pairs={{0,6},{1,13},{2,4},{3,15},{4,2},{5,9},{6,0},{7,11},{8,14},{9,5},{1... | collective-permute-start | bytes 442376 | tf_op jit(solution)/shard_map/ppermute | solution.py:224
  128.4 14.1 %collective-permute-start.52 = (bf16[2,9,32,128]{3,2,1,0:T(8,128)(2,1)S(1)}, bf16[2,9,32,128]{3,2,1,0:T(8,128)(2,1)S(1)}, u32[]{:S(2)}, u32[]{:S(2)}) collective-permute-start(bf16[2,9,32,128]{3,2,1,0:T(8,128)(2,1)S(1)} %get-tuple-element.113), channel_id=1, source_target_pairs={{0,12},{1,11},{2,14},{3,9},{4,8},{5,15},{6,10},{7,13},{8,4},{9,3},... | collective-permute-start | bytes 442376 | tf_op jit(solution)/shard_map/ppermute | solution.py:224
  128.8 13.7 %collective-permute-start.53 = (bf16[2,9,32,128]{3,2,1,0:T(8,128)(2,1)S(1)}, bf16[2,9,32,128]{3,2,1,0:T(8,128)(2,1)S(1)}, u32[]{:S(2)}, u32[]{:S(2)}) collective-permute-start(bf16[2,9,32,128]{3,2,1,0:T(8,128)(2,1)S(1)} %get-tuple-element.114), channel_id=1, source_target_pairs={{0,10},{1,7},{2,8},{3,5},{4,14},{5,3},{6,12},{7,1},{8,2},{9,15},{1... | collective-permute-start | bytes 442376 | tf_op jit(solution)/shard_map/ppermute | solution.py:224
  131.8 11.4 %collective-permute-start.54 = (bf16[2,9,32,128]{3,2,1,0:T(8,128)(2,1)S(1)}, bf16[2,9,32,128]{3,2,1,0:T(8,128)(2,1)S(1)}, u32[]{:S(2)}, u32[]{:S(2)}) collective-permute-start(bf16[2,9,32,128]{3,2,1,0:T(8,128)(2,1)S(1)} %get-tuple-element.115), channel_id=1, source_target_pairs={{0,2},{1,5},{2,0},{3,7},{4,6},{5,1},{6,4},{7,3},{8,10},{9,13},{10,... | collective-permute-start | bytes 442376 | tf_op jit(solution)/shard_map/ppermute | solution.py:224
  135.8 7.4 %collective-permute-start.55 = (bf16[2,9,32,128]{3,2,1,0:T(8,128)(2,1)S(1)}, bf16[2,9,32,128]{3,2,1,0:T(8,128)(2,1)S(1)}, u32[]{:S(2)}, u32[]{:S(2)}) collective-permute-start(bf16[2,9,32,128]{3,2,1,0:T(8,128)(2,1)S(1)} %get-tuple-element.116), channel_id=1, source_target_pairs={{0,4},{1,9},{2,6},{3,11},{4,0},{5,13},{6,2},{7,15},{8,12},{9,1},{1... | collective-permute-start | bytes 442376 | tf_op jit(solution)/shard_map/ppermute | solution.py:224
  142.5 5.5 %collective-permute-start.56 = (bf16[2,9,32,128]{3,2,1,0:T(8,128)(2,1)S(1)}, bf16[2,9,32,128]{3,2,1,0:T(8,128)(2,1)S(1)}, u32[]{:S(2)}, u32[]{:S(2)}) collective-permute-start(bf16[2,9,32,128]{3,2,1,0:T(8,128)(2,1)S(1)} %get-tuple-element.117), channel_id=1, source_target_pairs={{0,8},{1,3},{2,10},{3,1},{4,12},{5,7},{6,14},{7,5},{8,0},{9,11},{1... | collective-permute-start | bytes 442376 | tf_op jit(solution)/shard_map/ppermute | solution.py:224
  148.1 6.0 %collective-permute-start.57 = (bf16[9,32,128]{2,1,0:T(8,128)(2,1)S(1)}, bf16[9,32,128]{2,1,0:T(8,128)(2,1)S(1)}, u32[]{:S(2)}, u32[]{:S(2)}) collective-permute-start(bf16[9,32,128]{2,1,0:T(8,128)(2,1)S(1)} %get-tuple-element.119), channel_id=1, source_target_pairs={{0,16},{1,17},{2,18},{3,19},{4,20},{5,21},{6,22},{7,23},{8,24},{9,... | collective-permute-start | bytes 221192 | tf_op jit(solution)/shard_map/ppermute | solution.py:220
  148.2 1.2 collective-permute-start.38
  148.3 1.3 collective-permute-start.39
  (15 other events, 26.2 us)

commit v10 on v9

--- a/solution.py
+++ b/solution.py
@@ -86,25 +86,25 @@
     emit_coeffs(lambda i: v_ref[i], basis_ref, transfer_ref, ranks_ref, out_ref, leaves, rank_top)
 
 
-def couple_kernel(source_ref, target_ref, coupling_ref, *refs, order, unroll):
-    chips = sum(len(group) for group in order)
-    in_refs, out_refs, (sources, total) = refs[: 2 * chips], refs[2 * chips : -2], refs[-2:]
+def couple_kernel(source_ref, target_ref, coupling_ref, *refs, sets, unroll):
+    in_refs, out_refs, (sources, total) = refs[:sets], refs[sets:-2], refs[-2:]
     blocks, rank_top, _ = coupling_ref.shape
-    far, mains, rhs, _ = in_refs[0].shape
+    chips, far, mains, rhs, _ = in_refs[0].shape
     quads = mains // 3
     clusters = mains + quads
 
     def split(f, _):
         for n, packed_ref in enumerate(in_refs):
-            row = (n * far + f) * clusters
-            tiles = [packed_ref[f, c] for c in range(mains)]
-            for c in range(mains):
-                sources[row + c] = tiles[c]
-            for q in range(quads):
-                wide = [tile.astype(F32) for tile in tiles[3 * q : 3 * q + 3]]
-                sources[row + mains + q] = fourth(wide, rank_top).astype(BF)
-            for c in range(clusters):
-                total[row + c] = jnp.zeros((rhs, LANES), F32)
+            for chip in range(chips):
+                row = ((n * chips + chip) * far + f) * clusters
+                tiles = [packed_ref[chip, f, c] for c in range(mains)]
+                for c in range(mains):
+                    sources[row + c] = tiles[c]
+                for q in range(quads):
+                    wide = [tile.astype(F32) for tile in tiles[3 * q : 3 * q + 3]]
+                    sources[row + mains + q] = fourth(wide, rank_top).astype(BF)
+                for c in range(clusters):
+                    total[row + c] = jnp.zeros((rhs, LANES), F32)
         return 0
 
     lax.fori_loop(0, far, split, 0)
@@ -120,14 +120,13 @@
     lax.fori_loop(0, blocks // unroll, some, 0)
 
     def pack(f, _):
-        for core in range(2):
-            for g, group in enumerate(order):
-                for place, chip in enumerate(group):
-                    row = ((core * chips + chip) * far + f) * clusters
-                    for q in range(quads):
-                        mains_now = [total[row + 3 * q + k] for k in range(3)]
-                        for k, tile in enumerate(packed(mains_now, total[row + mains + q], rank_top)):
-                            out_refs[core * len(order) + g][place, f, 3 * q + k] = tile.astype(BF)
+        for n, packed_ref in enumerate(out_refs):
+            for chip in range(chips):
+                row = ((n * chips + chip) * far + f) * clusters
+                for q in range(quads):
+                    mains_now = [total[row + 3 * q + k] for k in range(3)]
+                    for k, tile in enumerate(packed(mains_now, total[row + mains + q], rank_top)):
+                        packed_ref[chip, f, 3 * q + k] = tile.astype(BF)
         return 0
 
     lax.fori_loop(0, far, pack, 0)
@@ -151,32 +150,39 @@
     out_ref[1] = dot(jnp.where(even, inner, outer), last_ref[0, 0])
 
 
-def add_kernel(keep_ref, swap_ref, *out_refs):
-    for n, out_ref in enumerate(out_refs):
-        out_ref[...] = (keep_ref[n].astype(F32) + swap_ref[n].astype(F32)).astype(out_ref.dtype)
-
-
-def last_add_kernel(own_ref, *refs, parts):
-    part_refs, (keep_out, *away_refs) = refs[:parts], refs[parts:]
-    for f in range(own_ref.shape[0]):
-        total = own_ref[f]
+def join_kernel(*refs):
+    for n, part_ref in enumerate(refs[:-1]):
+        refs[-1][n] = part_ref[...]
+
+
+def halve_kernel(*refs, parts):
+    part_refs, (keep_out, *send_refs) = refs[:parts], refs[parts:]
+    pieces = 1 + len(send_refs)
+    size = part_refs[0].shape[0] // pieces
+    for n in range(pieces):
+        total = None
         for part_ref in part_refs:
-            total = total + part_ref[f].astype(F32)
-        if f == 0:
+            part = part_ref[pl.ds(n * size, size)].astype(F32)
+            total = part if total is None else total + part
+        if n == 0:
             keep_out[...] = total
         else:
-            away_refs[f - 1][...] = total.astype(BF)
+            send_refs[n - 1][...] = total.astype(BF)
+
+
+def add_kernel(first_ref, second_ref, out_ref):
+    out_ref[...] = (first_ref[...].astype(F32) + second_ref[...].astype(F32)).astype(BF)
 
 
 def field_kernel(ranks_ref, core_ref, near_ref, edge_ref, basis_ref, transfer_ref, keep_ref, *rest, away):
     term_refs, out_ref, next_refs = rest[:away], rest[away], rest[away + 1 :]
     leaves, rank_top, _ = basis_ref.shape
-    mains, rhs, _ = keep_ref.shape
+    _, mains, rhs, _ = keep_ref.shape
     tiles = []
     for t in range(mains):
-        tile = keep_ref[t]
+        tile = keep_ref[0, t]
         for term_ref in term_refs:
-            tile = tile + term_ref[t].astype(F32)
+            tile = tile + term_ref[0, t].astype(F32)
         tiles.append(tile)
     sums = tiles + [fourth(tiles[3 * q : 3 * q + 3], rank_top) for q in range(mains // 3)]
     lane = lax.broadcasted_iota(jnp.int32, (rhs, rank_top), 1)
@@ -261,12 +267,13 @@
         ],
     )(ranks, core_index, charges, basis, transfer)
 
-    order = ((x | y | z, x | y, y | z, z | x), (0, x, y, z))
+    sets = cores * 2
+    half_shape = shape((chips // 2, far) + tile_shape, BF)
     couple = pl.pallas_call(
-        functools.partial(couple_kernel, order=order, unroll=8),
-        out_shape=[shape((4, far) + tile_shape, BF)] * 4,
-        in_specs=[SMEM, SMEM, VMEM] + [VMEM] * (cores * chips),
-        out_specs=[VMEM] * 4,
+        functools.partial(couple_kernel, sets=sets, unroll=8),
+        out_shape=[half_shape] * sets,
+        in_specs=[SMEM, SMEM, VMEM] + [VMEM] * sets,
+        out_specs=[VMEM] * sets,
         scratch_shapes=[
             pltpu.VMEM((devices * clusters, rhs, LANES), BF),
             pltpu.VMEM((devices * clusters, rhs, LANES), F32),
@@ -303,23 +310,23 @@
         compiler_params=params(16),
     )
 
-    def adder(kernel, inputs, outputs):
+    def call(kernel, outputs, *args):
         return pl.pallas_call(
             kernel,
             out_shape=outputs,
-            in_specs=[VMEM] * inputs,
+            in_specs=[VMEM] * len(args),
             out_specs=[VMEM] * len(outputs),
             compiler_params=params(16),
-        )
-
-    own_shape = shape((far,) + tile_shape, F32)
-    far_add = adder(add_kernel, 2, [part_shape] * 4)
-    near_add = adder(add_kernel, 2, [own_shape] + [part_shape] * 3)
-    last_add = adder(
-        functools.partial(last_add_kernel, parts=chips - 1),
-        chips,
-        [shape(tile_shape, F32)] + [tile_out] * (far - 1),
-    )
+        )(*args)
+
+    def join(*parts):
+        return call(join_kernel, [shape((len(parts),) + parts[0].shape, BF)], *parts)[0]
+
+    def halve(pieces, *parts):
+        lead = parts[0].shape[0] // pieces
+        sizes = (lead,) + parts[0].shape[1:]
+        outputs = [shape(sizes, F32)] + [shape(sizes, BF)] * (pieces - 1)
+        return call(functools.partial(halve_kernel, parts=len(parts)), outputs, *parts)
 
     def finish(with_coeffs):
         return pl.pallas_call(
@@ -333,44 +340,48 @@
     halo_pairs = [(d, d + cores) for d in range(1, devices - cores, cores)]
     halo_pairs += [(d, d - cores) for d in range(cores, devices, cores)]
 
-    long, short = order[0], order[1][1:]
-
     def apply_matrix(field_in, coeffs, inner, outer, coupling, with_coeffs):
+        early = coupling is not given
         away = [swap_far(coeffs, s) for s in range(1, far)]
-        outer = lax.ppermute(outer, "clu", halo_pairs)
-        away, outer, coupling = barrier((away, outer, coupling))
-        column = jnp.stack([coeffs] + away)
-        got = {chip: swap(column, chip) for chip in long + short}
-        near_sum = near(field_in, near_field)
-        got, near_sum = barrier((got, near_sum))
-        got[0] = column
-        other = {chip: swap_cores(got[chip]) for chip in got}
-        keep_long, keep, send_long, send = couple(
-            source_rows,
-            target_rows,
-            coupling,
-            *[got[chip] for chip in range(chips)],
-            *[other[chip] for chip in range(chips)],
-        )
-        parts = far_add(keep_long, swap_cores(send_long))
-        own, *rest = near_add(keep, swap_cores(send))
-        parts = [swap(part, chip) for part, chip in zip([*parts, *rest], long + short)]
-        total, *away = last_add(own, *parts)
-        terms = [swap_far(part, s + 1) for s, part in enumerate(away)]
+        if not early:
+            outer = lax.ppermute(outer, "clu", halo_pairs)
+            near_sum = near(field_in, near_field)
+            away, outer, near_sum = barrier((away, outer, near_sum))
+            coupling = relaid
+        column = join(coeffs, *away)
+        square = join(column, swap(column, x))
+        square = join(square, swap(square, y)).reshape(half_shape.shape)
+        if early:
+            square, outer = barrier((square, outer))
+            outer = lax.ppermute(outer, "clu", halo_pairs)
+            near_sum = near(field_in, near_field)
+        beyond, other, coupling, near_sum = barrier((swap(square, z), swap_cores(square), coupling, near_sum))
+        other_beyond, outer = barrier((swap_cores(beyond), outer))
+        totals = couple(source_rows, target_rows, coupling, square, beyond, other, other_beyond)
+        keep, keep_beyond, send, send_beyond = totals
+        (sent,) = call(add_kernel, [half_shape], keep_beyond, swap_cores(send_beyond))
+        sent, send = barrier((sent, send))
         inner, outer = swap_cores(inner), swap_cores(outer)
         edges = edge(core_index, inner, outer, near_field, near_field)
+        sent, swapped, edges = barrier((swap(sent, z), swap_cores(send), edges))
+        keep, sent = halve(2, *[part.reshape((2, 2 * far) + tile_shape) for part in (keep, swapped, sent)])
+        keep, sent = halve(2, *[part.reshape((2, far) + tile_shape) for part in (keep, swap(sent, y))])
+        total, *away = halve(far, *[part.reshape((far,) + tile_shape) for part in (keep, swap(sent, x))])
+        terms = [swap_far(part, s + 1) for s, part in enumerate(away)]
         return finish(with_coeffs)(ranks, core_index, near_sum, edges, basis, transfer, total, *terms)
 
+    given = coupling
     coupling, first_coeffs = barrier((coupling, first_coeffs))
-    coupling = pl.pallas_call(
+    relaid = pl.pallas_call(
         lambda in_ref, out_ref: None,
         out_shape=shape(coupling.shape, BF),
         in_specs=[pl.BlockSpec(memory_space=pl.ANY)],
         out_specs=pl.BlockSpec(memory_space=pl.ANY),
         input_output_aliases={0: 0},
+        compiler_params=params(1),
     )(coupling)
-    first, *second_args = apply_matrix(charges, first_coeffs, inner, outer, coupling, True)
-    (second,) = apply_matrix(first, *second_args, coupling, False)
+    first, *second_args = apply_matrix(charges, first_coeffs, inner, outer, given, True)
+    (second,) = apply_matrix(first, *second_args, relaid, False)
     return (first, second)
 
 

time: 157 us -> 151 us (0.962)
  waiting for transfers between devices: 58.6 us -> 80.8 us
  starting transfers between devices: 60.2 us -> 38.9 us
  local copies, waits for them, and re-layouts: 14.6 us -> 7.26 us
  Pallas kernels: 21.5 us -> 23.1 us
    ppermute x28 -> x12, starting transfers between devices: 42.8 us -> 21.8 us  [swap(): lax.ppermute(part, 'clu', [(d, d ^ (turned if d % cores else direction) *...]
    ppermute x28 -> x12, waiting for transfers between devices: 39.1 us -> 59 us  [swap(): lax.ppermute(part, 'clu', [(d, d ^ (turned if d % cores else direction) *...]
    unnamed x42 -> x22, local copies, waits for them, and re-layouts: 9.78 us -> 3.73 us
    ppermute x24 -> x12, starting transfers between devices: 5.15 us -> 1.44 us  [swap_cores(): return lax.ppermute(part, 'clu', [(d, d ^ 1) for d in range(devices)])]
    ppermute x4, starting transfers between devices: 9.7 us -> 13.1 us  [swap_far(): lax.ppermute(part, 'clu', [(d, (d + shift * cube) % devices) for d in ran...]
    ppermute x24 -> x12, waiting for transfers between devices: 7.54 us -> 9.16 us  [swap_cores(): return lax.ppermute(part, 'clu', [(d, d ^ 1) for d in range(devices)])]
    pallas_call x8 -> x16, Pallas kernels: 12.2 us -> 13.8 us  [the longest x2 11.9 us: apply_matrix(): couple(source_rows, target_rows, coupling, square, beyond, other, other_b...]
  transfers between devices with their start and end apart: 58 -> 30, of which waited for: 31 -> 22; matrix products, arithmetic and copies ran while one was open for 4% -> 2% of each run, Pallas kernels for 1% -> 1%
where the time goes in v10:
time: 151 us
  waiting for transfers between devices  80.8 us (54%)
  starting transfers between devices  38.9 us (26%)
  Pallas kernels  23.1 us (15%)
  local copies, waits for them, and re-layouts  7.26 us (5%)
    ppermute x12, waiting for transfers between devices, swap(): lax.ppermute(part, 'clu', [(d, d ^ (turned if d % cores else direction) *...  59 us
    ppermute x12, starting transfers between devices, swap(): lax.ppermute(part, 'clu', [(d, d ^ (turned if d % cores else direction) *...  21.8 us
    ppermute x4, starting transfers between devices, swap_far(): lax.ppermute(part, 'clu', [(d, (d + shift * cube) % devices) for d in ran...  13.1 us
    pallas_call x2, Pallas kernels, apply_matrix(): couple(source_rows, target_rows, coupling, square, beyond, other, other_b...  11.9 us
    ppermute x12, waiting for transfers between devices, swap_cores(): return lax.ppermute(part, 'clu', [(d, d ^ 1) for d in range(devices)])  9.16 us
    ppermute x4, waiting for transfers between devices, swap_far(): lax.ppermute(part, 'clu', [(d, (d + shift * cube) % devices) for d in ran...  7.03 us
    ppermute x2, waiting for transfers between devices, apply_matrix(): outer = lax.ppermute(outer, 'clu', halo_pairs)  5.65 us
    pallas_call x2, Pallas kernels, apply_matrix(): finish(with_coeffs)  4.98 us
  transfers between devices with their start and end apart: 30, of which 22 were waited for; matrix products, arithmetic and copies ran while one was open for 2% of the time, Pallas kernels for 1%

profile of v10, /device:TPU:0, one launch (start us, length us, event | category | flops | bytes accessed | tf_op | source)
XLA Modules:
  0.0 151.0 jit_solution(13217895814469032790)
XLA Ops:
  0.6 2.9 %shard_map.95 = (bf16[9,32,128]{2,1,0:T(8,128)(2,1)}, bf16[1,32,256]{2,1,0:T(8,128)(2,1)}, bf16[1,32,256]{2,1,0:T(8,128)(2,1)}) custom-call(s32[12]{0:T(128)} %ranks_ref.5, s32[1]{0:T(128)} %bitcast.core_ref, bf16[8,32,256]{2,1,0:T(8,128)(2,1)} %v_ref.1, bf16[8,96,256]{2,1,0:T(8,128)(2,1)} %basis_ref.3, bf16[8,96,96]{2,1,0:T(8,128)(2,1)} %transfer_ref.3), custom_call_target="tpu_custom_call" | custom-call | tf_op jit(solution)/shard_map/pallas_call | solution.py:257
  3.5 4.1 %collective-permute-start = (bf16[9,32,128]{2,1,0:T(8,128)(2,1)}, bf16[9,32,128]{2,1,0:T(8,128)(2,1)S(1)}, u32[]{:S(2)}, u32[]{:S(2)}) collective-permute-start(bf16[9,32,128]{2,1,0:T(8,128)(2,1)} %get-tuple-element.59.refs_0_), channel_id=1, source_target_pairs={{0,16},{1,17},{2,18},{3,19},{4,20},{5,21},{6,22},{7,23},{8,24},{9,... | collective-permute-start | bytes 221192 | tf_op jit(solution)/shard_map/ppermute | solution.py:226
  7.6 1.3 collective-permute-start.1
  8.9 1.9 %copy-done = bf16[8,3,256,256]{3,2,1,0:T(8,128)(2,1)S(1)} copy-done((bf16[8,3,256,256]{3,2,1,0:T(8,128)(2,1)S(1)}, bf16[8,3,256,256]{3,2,1,0:T(8,128)(2,1)}, u32[]{:S(2)}) %copy-start) | copy-done | bytes 3145752
  10.8 0.9 copy-done.4
  11.7 0.6 shard_map.96.near_ref
  12.3 1.1 collective-permute-done.1
  13.5 2.5 %collective-permute-start.2 = (bf16[2,9,32,128]{3,2,1,0:T(8,128)(2,1)S(1)}, bf16[2,9,32,128]{3,2,1,0:T(8,128)(2,1)S(1)}, u32[]{:S(2)}, u32[]{:S(2)}) collective-permute-start(bf16[2,9,32,128]{3,2,1,0:T(8,128)(2,1)S(1)} %shard_map.97.refs_0_), channel_id=1, source_target_pairs={{0,2},{1,5},{2,0},{3,7},{4,6},{5,1},{6,4},{7,3},{8,10},{9,13},{10,... | collective-permute-start | bytes 442376 | tf_op jit(solution)/shard_map/ppermute | solution.py:230
  16.0 3.1 %collective-permute-done.2.refs_1_ = bf16[2,9,32,128]{3,2,1,0:T(8,128)(2,1)S(1)} collective-permute-done((bf16[2,9,32,128]{3,2,1,0:T(8,128)(2,1)S(1)}, bf16[2,9,32,128]{3,2,1,0:T(8,128)(2,1)S(1)}, u32[]{:S(2)}, u32[]{:S(2)}) %collective-permute-start.2) | collective-permute-done | bytes 147488 | tf_op jit(solution)/shard_map/ppermute | solution.py:230
  19.1 2.5 %collective-permute-start.3 = (bf16[2,2,9,32,128]{4,3,2,1,0:T(8,128)(2,1)S(1)}, bf16[2,2,9,32,128]{4,3,2,1,0:T(8,128)(2,1)S(1)}, u32[]{:S(2)}, u32[]{:S(2)}) collective-permute-start(bf16[2,2,9,32,128]{4,3,2,1,0:T(8,128)(2,1)S(1)} %shard_map.98.refs_0_), channel_id=1, source_target_pairs={{0,4},{1,9},{2,6},{3,11},{4,0},{5,13},{6,2},{7,15},{8,12},{9,1},{1... | collective-permute-start | bytes 884744 | tf_op jit(solution)/shard_map/ppermute | solution.py:230
  21.6 4.7 %collective-permute-done.3.refs_1_ = bf16[2,2,9,32,128]{4,3,2,1,0:T(8,128)(2,1)S(1)} collective-permute-done((bf16[2,2,9,32,128]{4,3,2,1,0:T(8,128)(2,1)S(1)}, bf16[2,2,9,32,128]{4,3,2,1,0:T(8,128)(2,1)S(1)}, u32[]{:S(2)}, u32[]{:S(2)}) %collective-permute-start.3) | collective-permute-done | bytes 294944 | tf_op jit(solution)/shard_map/ppermute | solution.py:230
  26.3 0.9 shard_map.99
  27.1 2.9 %collective-permute-start.4 = (bf16[4,2,9,32,128]{4,3,2,1,0:T(8,128)(2,1)}, bf16[4,2,9,32,128]{4,3,2,1,0:T(8,128)(2,1)}, u32[]{:S(2)}, u32[]{:S(2)}) collective-permute-start(bf16[4,2,9,32,128]{4,3,2,1,0:T(8,128)(2,1)} %bitcast.1.refs_0_), channel_id=1, source_target_pairs={{0,8},{1,3},{2,10},{3,1},{4,12},{5,7},{6,14},{7,5},{8,0},{9,11},{1... | collective-permute-start | bytes 1769480 | tf_op jit(solution)/shard_map/ppermute | solution.py:230
  30.0 3.5 %copy.11.in_ref = bf16[128,96,96]{2,1,0:T(8,128)(2,1)S(1)} copy(bf16[128,96,96]{0,2,1:T(8,128)(2,1)} %param.12) | data formatting | bytes 4718592 | tf_op jit(solution)/shard_map/optimization_barrier | solution.py:374
  33.6 4.6 %collective-permute-done.4.refs_1_ = bf16[4,2,9,32,128]{4,3,2,1,0:T(8,128)(2,1)} collective-permute-done((bf16[4,2,9,32,128]{4,3,2,1,0:T(8,128)(2,1)}, bf16[4,2,9,32,128]{4,3,2,1,0:T(8,128)(2,1)}, u32[]{:S(2)}, u32[]{:S(2)}) %collective-permute-start.4) | collective-permute-done | bytes 589856 | tf_op jit(solution)/shard_map/ppermute | solution.py:230
  38.3 2.3 %collective-permute-done.6.refs_3_ = bf16[4,2,9,32,128]{4,3,2,1,0:T(8,128)(2,1)} collective-permute-done((bf16[4,2,9,32,128]{4,3,2,1,0:T(8,128)(2,1)}, bf16[4,2,9,32,128]{4,3,2,1,0:T(8,128)(2,1)}, u32[]{:S(2)}, u32[]{:S(2)}) %collective-permute-start.6) | collective-permute-done | bytes 589856 | tf_op jit(solution)/shard_map/ppermute | solution.py:235
  40.6 6.5 %shard_map.101 = (bf16[4,2,9,32,128]{4,3,2,1,0:T(8,128)(2,1)S(1)}, bf16[4,2,9,32,128]{4,3,2,1,0:T(8,128)(2,1)S(1)}, bf16[4,2,9,32,128]{4,3,2,1,0:T(8,128)(2,1)S(1)}, bf16[4,2,9,32,128]{4,3,2,1,0:T(8,128)(2,1)S(1)}) custom-call(s32[128]{0:T(128)S(1)} %get-tuple-element.114.source_ref, s32[128]{0:T(128)S(1)} %get-tuple-element.115.target_ref, ...), custom_call_target="tpu_custom_call" | custom-call | flops 75497472 | bytes 10485760 | tf_op jit(solution)/shard_map/pallas_call | solution.py:360
  47.1 0.2 collective-permute-start.7
  47.3 1.9 %collective-permute-done.7.second_ref = bf16[4,2,9,32,128]{4,3,2,1,0:T(8,128)(2,1)S(1)} collective-permute-done((bf16[4,2,9,32,128]{4,3,2,1,0:T(8,128)(2,1)S(1)}, bf16[4,2,9,32,128]{4,3,2,1,0:T(8,128)(2,1)S(1)}, u32[]{:S(2)}, u32[]{:S(2)}) %collective-permute-start.7) | collective-permute-done | bytes 589856 | tf_op jit(solution)/shard_map/ppermute | solution.py:235
  49.2 0.1 shard_map.102
  49.3 2.1 %collective-permute-start.8 = (bf16[4,2,9,32,128]{4,3,2,1,0:T(8,128)(2,1)S(1)}, bf16[4,2,9,32,128]{4,3,2,1,0:T(8,128)(2,1)S(1)}, u32[]{:S(2)}, u32[]{:S(2)}) collective-permute-start(bf16[4,2,9,32,128]{4,3,2,1,0:T(8,128)(2,1)S(1)} %shard_map.102), channel_id=1, source_target_pairs={{0,8},{1,3},{2,10},{3,1},{4,12},{5,7},{6,14},{7,5},{8,0},{9,11},{1... | collective-permute-start | bytes 1769480 | tf_op jit(solution)/shard_map/ppermute | solution.py:230
  51.4 0.5 collective-permute-start.10
  51.9 0.1 collective-permute-start.11
  52.0 1.4 collective-permute-done.10.inner_ref
  53.5 0.1 shard_map.103.edge_ref
  53.6 5.6 %collective-permute-done.8 = bf16[4,2,9,32,128]{4,3,2,1,0:T(8,128)(2,1)S(1)} collective-permute-done((bf16[4,2,9,32,128]{4,3,2,1,0:T(8,128)(2,1)S(1)}, bf16[4,2,9,32,128]{4,3,2,1,0:T(8,128)(2,1)S(1)}, u32[]{:S(2)}, u32[]{:S(2)}) %collective-permute-start.8) | collective-permute-done | bytes 589856 | tf_op jit(solution)/shard_map/ppermute | solution.py:230
  59.3 0.2 shard_map.104
  59.5 1.2 collective-permute-start.12
  60.7 5.6 %collective-permute-done.12 = bf16[1,4,9,32,128]{4,3,2,1,0:T(8,128)(2,1)S(1)} collective-permute-done((bf16[1,4,9,32,128]{4,3,2,1,0:T(8,128)(2,1)S(1)}, bf16[1,4,9,32,128]{4,3,2,1,0:T(8,128)(2,1)S(1)}, u32[]{:S(2)}, u32[]{:S(2)}) %collective-permute-start.12) | collective-permute-done | bytes 294944 | tf_op jit(solution)/shard_map/ppermute | solution.py:230
  66.4 1.2 collective-permute-start.13
  67.6 4.0 %collective-permute-done.13 = bf16[1,2,9,32,128]{4,3,2,1,0:T(8,128)(2,1)S(1)} collective-permute-done((bf16[1,2,9,32,128]{4,3,2,1,0:T(8,128)(2,1)S(1)}, bf16[1,2,9,32,128]{4,3,2,1,0:T(8,128)(2,1)S(1)}, u32[]{:S(2)}, u32[]{:S(2)}) %collective-permute-start.13) | collective-permute-done | bytes 147488 | tf_op jit(solution)/shard_map/ppermute | solution.py:230
  71.6 3.1 %collective-permute-start.14 = (bf16[1,9,32,128]{3,2,1,0:T(8,128)(2,1)S(1)}, bf16[1,9,32,128]{3,2,1,0:T(8,128)(2,1)S(1)}, u32[]{:S(2)}, u32[]{:S(2)}) collective-permute-start(bf16[1,9,32,128]{3,2,1,0:T(8,128)(2,1)S(1)} %get-tuple-element.86), channel_id=1, source_target_pairs={{0,16},{1,17},{2,18},{3,19},{4,20},{5,21},{6,22},{7,23},{8,24},{9,... | collective-permute-start | bytes 221192 | tf_op jit(solution)/shard_map/ppermute | solution.py:226
  74.7 2.3 %collective-permute-done.14.rest_0_ = bf16[1,9,32,128]{3,2,1,0:T(8,128)(2,1)S(1)} collective-permute-done((bf16[1,9,32,128]{3,2,1,0:T(8,128)(2,1)S(1)}, bf16[1,9,32,128]{3,2,1,0:T(8,128)(2,1)S(1)}, u32[]{:S(2)}, u32[]{:S(2)}) %collective-permute-start.14) | collective-permute-done | bytes 73760 | tf_op jit(solution)/shard_map/ppermute | solution.py:226
  77.1 2.5 %shard_map.107 = (bf16[8,32,256]{2,1,0:T(8,128)(2,1)}, bf16[9,32,128]{2,1,0:T(8,128)(2,1)S(1)}, bf16[1,32,256]{2,1,0:T(8,128)(2,1)S(1)}, bf16[1,32,256]{2,1,0:T(8,128)(2,1)S(1)}) custom-call(s32[12]{0:T(128)S(1)} %copy-done.7, s32[1]{0:T(128)} %bitcast.core_ref, f32[8,32,256]{2,1,0:T(8,128)S(1)} %shard_map.96.near_ref, ...), custom_call_target="tpu_custom_call" | custom-call | tf_op jit(solution)/shard_map/pallas_call | solution.py:371
  79.6 2.9 %collective-permute-start.15 = (bf16[9,32,128]{2,1,0:T(8,128)(2,1)S(1)}, bf16[9,32,128]{2,1,0:T(8,128)(2,1)S(1)}, u32[]{:S(2)}, u32[]{:S(2)}) collective-permute-start(bf16[9,32,128]{2,1,0:T(8,128)(2,1)S(1)} %get-tuple-element.88.refs_0_), channel_id=1, source_target_pairs={{0,16},{1,17},{2,18},{3,19},{4,20},{5,21},{6,22},{7,23},{8,24},{9,... | collective-permute-start | bytes 221192 | tf_op jit(solution)/shard_map/ppermute | solution.py:226
  82.5 2.3 %collective-permute-done.15.refs_1_ = bf16[9,32,128]{2,1,0:T(8,128)(2,1)S(1)} collective-permute-done((bf16[9,32,128]{2,1,0:T(8,128)(2,1)S(1)}, bf16[9,32,128]{2,1,0:T(8,128)(2,1)S(1)}, u32[]{:S(2)}, u32[]{:S(2)}) %collective-permute-start.15) | collective-permute-done | bytes 73760 | tf_op jit(solution)/shard_map/ppermute | solution.py:226
  84.8 1.1 collective-permute-start.16
  85.9 4.1 %collective-permute-done.16.refs_1_ = bf16[2,9,32,128]{3,2,1,0:T(8,128)(2,1)S(1)} collective-permute-done((bf16[2,9,32,128]{3,2,1,0:T(8,128)(2,1)S(1)}, bf16[2,9,32,128]{3,2,1,0:T(8,128)(2,1)S(1)}, u32[]{:S(2)}, u32[]{:S(2)}) %collective-permute-start.16) | collective-permute-done | bytes 147488 | tf_op jit(solution)/shard_map/ppermute | solution.py:230
  90.1 1.1 collective-permute-start.17
  91.2 5.7 %collective-permute-done.17.refs_1_ = bf16[2,2,9,32,128]{4,3,2,1,0:T(8,128)(2,1)S(1)} collective-permute-done((bf16[2,2,9,32,128]{4,3,2,1,0:T(8,128)(2,1)S(1)}, bf16[2,2,9,32,128]{4,3,2,1,0:T(8,128)(2,1)S(1)}, u32[]{:S(2)}, u32[]{:S(2)}) %collective-permute-start.17) | collective-permute-done | bytes 294944 | tf_op jit(solution)/shard_map/ppermute | solution.py:230
  96.9 0.1 collective-permute-start.19
  97.0 2.0 %collective-permute-start.18 = (bf16[4,2,9,32,128]{4,3,2,1,0:T(8,128)(2,1)S(1)}, bf16[4,2,9,32,128]{4,3,2,1,0:T(8,128)(2,1)S(1)}, u32[]{:S(2)}, u32[]{:S(2)}) collective-permute-start(bf16[4,2,9,32,128]{4,3,2,1,0:T(8,128)(2,1)S(1)} %bitcast.18), channel_id=1, source_target_pairs={{0,8},{1,3},{2,10},{3,1},{4,12},{5,7},{6,14},{7,5},{8,0},{9,11},{1... | collective-permute-start | bytes 1769480 | tf_op jit(solution)/shard_map/ppermute | solution.py:230
  99.0 0.9 copy-done.5
  99.9 0.6 shard_map.111.near_ref
  100.5 6.5 %collective-permute-done.18.refs_1_ = bf16[4,2,9,32,128]{4,3,2,1,0:T(8,128)(2,1)S(1)} collective-permute-done((bf16[4,2,9,32,128]{4,3,2,1,0:T(8,128)(2,1)S(1)}, bf16[4,2,9,32,128]{4,3,2,1,0:T(8,128)(2,1)S(1)}, u32[]{:S(2)}, u32[]{:S(2)}) %collective-permute-start.18) | collective-permute-done | bytes 589856 | tf_op jit(solution)/shard_map/ppermute | solution.py:230
  106.9 1.3 collective-permute-start.21
  108.2 4.5 %collective-permute-done.21 = bf16[1,32,256]{2,1,0:T(8,128)(2,1)S(1)} collective-permute-done((bf16[1,32,256]{2,1,0:T(8,128)(2,1)S(1)}, bf16[1,32,256]{2,1,0:T(8,128)(2,1)S(1)}, u32[]{:S(2)}, u32[]{:S(2)}) %collective-permute-start.21) | collective-permute-done | bytes 16416 | tf_op jit(solution)/shard_map/ppermute | solution.py:356
  112.7 5.3 %shard_map.112 = (bf16[4,2,9,32,128]{4,3,2,1,0:T(8,128)(2,1)S(1)}, bf16[4,2,9,32,128]{4,3,2,1,0:T(8,128)(2,1)S(1)}, bf16[4,2,9,32,128]{4,3,2,1,0:T(8,128)(2,1)S(1)}, bf16[4,2,9,32,128]{4,3,2,1,0:T(8,128)(2,1)S(1)}) custom-call(s32[128]{0:T(128)S(1)} %get-tuple-element.114.source_ref, s32[128]{0:T(128)S(1)} %get-tuple-element.115.target_ref, ...), custom_call_target="tpu_custom_call" | custom-call | flops 75497472 | bytes 10485760 | tf_op jit(solution)/shard_map/pallas_call | solution.py:360
  118.1 0.1 collective-permute-start.22
  118.1 2.0 %collective-permute-done.22.second_ref = bf16[4,2,9,32,128]{4,3,2,1,0:T(8,128)(2,1)S(1)} collective-permute-done((bf16[4,2,9,32,128]{4,3,2,1,0:T(8,128)(2,1)S(1)}, bf16[4,2,9,32,128]{4,3,2,1,0:T(8,128)(2,1)S(1)}, u32[]{:S(2)}, u32[]{:S(2)}) %collective-permute-start.22) | collective-permute-done | bytes 589856 | tf_op jit(solution)/shard_map/ppermute | solution.py:235
  120.1 0.2 shard_map.113
  120.3 2.6 %collective-permute-start.23 = (bf16[4,2,9,32,128]{4,3,2,1,0:T(8,128)(2,1)S(1)}, bf16[4,2,9,32,128]{4,3,2,1,0:T(8,128)(2,1)S(1)}, u32[]{:S(2)}, u32[]{:S(2)}) collective-permute-start(bf16[4,2,9,32,128]{4,3,2,1,0:T(8,128)(2,1)S(1)} %shard_map.113), channel_id=1, source_target_pairs={{0,8},{1,3},{2,10},{3,1},{4,12},{5,7},{6,14},{7,5},{8,0},{9,11},{1... | collective-permute-start | bytes 1769480 | tf_op jit(solution)/shard_map/ppermute | solution.py:230
  122.9 0.5 collective-permute-start.25
  123.4 1.5 %collective-permute-done.25.inner_ref = bf16[1,32,256]{2,1,0:T(8,128)(2,1)S(1)} collective-permute-done((bf16[1,32,256]{2,1,0:T(8,128)(2,1)S(1)}, bf16[1,32,256]{2,1,0:T(8,128)(2,1)S(1)}, u32[]{:S(2)}, u32[]{:S(2)}) %collective-permute-start.25) | collective-permute-done | bytes 16416 | tf_op jit(solution)/shard_map/ppermute | solution.py:235
  124.9 0.1 shard_map.114.edge_ref
  125.1 5.7 %collective-permute-done.23 = bf16[4,2,9,32,128]{4,3,2,1,0:T(8,128)(2,1)S(1)} collective-permute-done((bf16[4,2,9,32,128]{4,3,2,1,0:T(8,128)(2,1)S(1)}, bf16[4,2,9,32,128]{4,3,2,1,0:T(8,128)(2,1)S(1)}, u32[]{:S(2)}, u32[]{:S(2)}) %collective-permute-start.23) | collective-permute-done | bytes 589856 | tf_op jit(solution)/shard_map/ppermute | solution.py:230
  130.8 0.2 shard_map.115
  131.0 0.5 collective-permute-start.27
  131.5 6.3 %collective-permute-done.27 = bf16[1,4,9,32,128]{4,3,2,1,0:T(8,128)(2,1)S(1)} collective-permute-done((bf16[1,4,9,32,128]{4,3,2,1,0:T(8,128)(2,1)S(1)}, bf16[1,4,9,32,128]{4,3,2,1,0:T(8,128)(2,1)S(1)}, u32[]{:S(2)}, u32[]{:S(2)}) %collective-permute-start.27) | collective-permute-done | bytes 294944 | tf_op jit(solution)/shard_map/ppermute | solution.py:230
  137.8 2.2 %collective-permute-start.28 = (bf16[1,2,9,32,128]{4,3,2,1,0:T(8,128)(2,1)S(1)}, bf16[1,2,9,32,128]{4,3,2,1,0:T(8,128)(2,1)S(1)}, u32[]{:S(2)}, u32[]{:S(2)}) collective-permute-start(bf16[1,2,9,32,128]{4,3,2,1,0:T(8,128)(2,1)S(1)} %get-tuple-element.111), channel_id=1, source_target_pairs={{0,2},{1,5},{2,0},{3,7},{4,6},{5,1},{6,4},{7,3},{8,10},{9,13},{10,... | collective-permute-start | bytes 442376 | tf_op jit(solution)/shard_map/ppermute | solution.py:230
  140.1 3.1 %collective-permute-done.28 = bf16[1,2,9,32,128]{4,3,2,1,0:T(8,128)(2,1)S(1)} collective-permute-done((bf16[1,2,9,32,128]{4,3,2,1,0:T(8,128)(2,1)S(1)}, bf16[1,2,9,32,128]{4,3,2,1,0:T(8,128)(2,1)S(1)}, u32[]{:S(2)}, u32[]{:S(2)}) %collective-permute-start.28) | collective-permute-done | bytes 147488 | tf_op jit(solution)/shard_map/ppermute | solution.py:230
  143.2 3.0 %collective-permute-start.29 = (bf16[1,9,32,128]{3,2,1,0:T(8,128)(2,1)S(1)}, bf16[1,9,32,128]{3,2,1,0:T(8,128)(2,1)S(1)}, u32[]{:S(2)}, u32[]{:S(2)}) collective-permute-start(bf16[1,9,32,128]{3,2,1,0:T(8,128)(2,1)S(1)} %get-tuple-element.113), channel_id=1, source_target_pairs={{0,16},{1,17},{2,18},{3,19},{4,20},{5,21},{6,22},{7,23},{8,24},{9,... | collective-permute-start | bytes 221192 | tf_op jit(solution)/shard_map/ppermute | solution.py:226
  146.2 2.4 %collective-permute-done.29.rest_0_ = bf16[1,9,32,128]{3,2,1,0:T(8,128)(2,1)S(1)} collective-permute-done((bf16[1,9,32,128]{3,2,1,0:T(8,128)(2,1)S(1)}, bf16[1,9,32,128]{3,2,1,0:T(8,128)(2,1)S(1)}, u32[]{:S(2)}, u32[]{:S(2)}) %collective-permute-start.29) | collective-permute-done | bytes 73760 | tf_op jit(solution)/shard_map/ppermute | solution.py:226
  148.5 2.5 %shard_map.118 = bf16[8,32,256]{2,1,0:T(8,128)(2,1)} custom-call(s32[12]{0:T(128)S(1)} %copy-done.7, s32[1]{0:T(128)} %bitcast.core_ref, f32[8,32,256]{2,1,0:T(8,128)S(1)} %shard_map.111.near_ref, f32[2,32,256]{2,1,0:T(8,128)S(1)} %shard_map.114.edge_ref, bf16[8,96,256]{2,1,0:T(8,128)(2,1)S(1)} %copy-done.2, bf16[8,96,96]{2,1,0:T(8,128)(2,1)S(1)} %copy-done.3, ...), custom_call_target="tpu_custom_call" | custom-call | tf_op jit(solution)/shard_map/pallas_call | solution.py:371
  (44 shorter events, 0.4 us)
Async XLA Ops:
  3.5 9.9 %collective-permute-start = (bf16[9,32,128]{2,1,0:T(8,128)(2,1)}, bf16[9,32,128]{2,1,0:T(8,128)(2,1)S(1)}, u32[]{:S(2)}, u32[]{:S(2)}) collective-permute-start(bf16[9,32,128]{2,1,0:T(8,128)(2,1)} %get-tuple-element.59.refs_0_), channel_id=1, source_target_pairs={{0,16},{1,17},{2,18},{3,19},{4,20},{5,21},{6,22},{7,23},{8,24},{9,... | collective-permute-start | bytes 221192 | tf_op jit(solution)/shard_map/ppermute | solution.py:226
  7.6 5.8 %collective-permute-start.1 = (bf16[1,32,256]{2,1,0:T(8,128)(2,1)}, bf16[1,32,256]{2,1,0:T(8,128)(2,1)S(1)}, u32[]{:S(2)}, u32[]{:S(2)}) collective-permute-start(bf16[1,32,256]{2,1,0:T(8,128)(2,1)} %get-tuple-element.60), channel_id=1, source_target_pairs={{1,3},{3,5},{5,7},{7,9},{9,11},{11,13},{13,15},{15,17},{17,19},{19... | collective-permute-start | bytes 49160 | tf_op jit(solution)/shard_map/ppermute | solution.py:347
  8.9 1.9 %copy-start = (bf16[8,3,256,256]{3,2,1,0:T(8,128)(2,1)S(1)}, bf16[8,3,256,256]{3,2,1,0:T(8,128)(2,1)}, u32[]{:S(2)}) copy-start(bf16[8,3,256,256]{3,2,1,0:T(8,128)(2,1)} %last_ref.3) | copy-start | bytes 9437188
  10.8 0.9 copy-start.4
  11.7 1.8 %copy-start.6 = (bf16[9,32,128]{2,1,0:T(8,128)(2,1)S(1)}, bf16[9,32,128]{2,1,0:T(8,128)(2,1)}, u32[]{:S(2)}) copy-start(bf16[9,32,128]{2,1,0:T(8,128)(2,1)} %get-tuple-element.59.refs_0_) | copy-start | bytes 221188
  13.5 5.6 %collective-permute-start.2 = (bf16[2,9,32,128]{3,2,1,0:T(8,128)(2,1)S(1)}, bf16[2,9,32,128]{3,2,1,0:T(8,128)(2,1)S(1)}, u32[]{:S(2)}, u32[]{:S(2)}) collective-permute-start(bf16[2,9,32,128]{3,2,1,0:T(8,128)(2,1)S(1)} %shard_map.97.refs_0_), channel_id=1, source_target_pairs={{0,2},{1,5},{2,0},{3,7},{4,6},{5,1},{6,4},{7,3},{8,10},{9,13},{10,... | collective-permute-start | bytes 442376 | tf_op jit(solution)/shard_map/ppermute | solution.py:230
  19.1 7.2 %collective-permute-start.3 = (bf16[2,2,9,32,128]{4,3,2,1,0:T(8,128)(2,1)S(1)}, bf16[2,2,9,32,128]{4,3,2,1,0:T(8,128)(2,1)S(1)}, u32[]{:S(2)}, u32[]{:S(2)}) collective-permute-start(bf16[2,2,9,32,128]{4,3,2,1,0:T(8,128)(2,1)S(1)} %shard_map.98.refs_0_), channel_id=1, source_target_pairs={{0,4},{1,9},{2,6},{3,11},{4,0},{5,13},{6,2},{7,15},{8,12},{9,1},{1... | collective-permute-start | bytes 884744 | tf_op jit(solution)/shard_map/ppermute | solution.py:230
  27.1 6.5 %collective-permute-start.5 = (bf16[4,2,9,32,128]{4,3,2,1,0:T(8,128)(2,1)}, bf16[4,2,9,32,128]{4,3,2,1,0:T(8,128)(2,1)}, u32[]{:S(2)}, u32[]{:S(2)}) collective-permute-start(bf16[4,2,9,32,128]{4,3,2,1,0:T(8,128)(2,1)} %bitcast.1.refs_0_), channel_id=1, source_target_pairs={{0,1},{1,0},{2,3},{3,2},{4,5},{5,4},{6,7},{7,6},{8,9},{9,8},{10,11... | collective-permute-start | bytes 1769480 | tf_op jit(solution)/shard_map/ppermute | solution.py:235
  27.1 11.1 %collective-permute-start.4 = (bf16[4,2,9,32,128]{4,3,2,1,0:T(8,128)(2,1)}, bf16[4,2,9,32,128]{4,3,2,1,0:T(8,128)(2,1)}, u32[]{:S(2)}, u32[]{:S(2)}) collective-permute-start(bf16[4,2,9,32,128]{4,3,2,1,0:T(8,128)(2,1)} %bitcast.1.refs_0_), channel_id=1, source_target_pairs={{0,8},{1,3},{2,10},{3,1},{4,12},{5,7},{6,14},{7,5},{8,0},{9,11},{1... | collective-permute-start | bytes 1769480 | tf_op jit(solution)/shard_map/ppermute | solution.py:230
  33.6 4.6 %copy-start.8 = (s32[128]{0:T(128)S(1)}, s32[128]{0:T(128)}, u32[]{:S(2)}) copy-start(s32[128]{0:T(128)} %param.14) | copy-start | bytes 1540
  33.6 4.6 %copy-start.9 = (s32[128]{0:T(128)S(1)}, s32[128]{0:T(128)}, u32[]{:S(2)}) copy-start(s32[128]{0:T(128)} %param.15) | copy-start | bytes 1540
  38.2 2.3 %collective-permute-start.6 = (bf16[4,2,9,32,128]{4,3,2,1,0:T(8,128)(2,1)}, bf16[4,2,9,32,128]{4,3,2,1,0:T(8,128)(2,1)}, u32[]{:S(2)}, u32[]{:S(2)}) collective-permute-start(bf16[4,2,9,32,128]{4,3,2,1,0:T(8,128)(2,1)} %collective-permute-done.4.refs_1_), channel_id=1, source_target_pairs={{0,1},{1,0},{2,3},{3,2},{4,5},{5,4},{6,7},{7,6},{8,9},{9,8},{10,11... | collective-permute-start | bytes 1769480 | tf_op jit(solution)/shard_map/ppermute | solution.py:235
  40.6 10.9 %copy-start.10 = (bf16[1,32,256]{2,1,0:T(8,128)(2,1)S(1)}, bf16[1,32,256]{2,1,0:T(8,128)(2,1)}, u32[]{:S(2)}) copy-start(bf16[1,32,256]{2,1,0:T(8,128)(2,1)} %get-tuple-element.75) | copy-start | bytes 49156
  40.6 12.9 %copy-start.1 = (bf16[8,3,256,256]{3,2,1,0:T(8,128)(2,1)S(1)}, bf16[8,3,256,256]{3,2,1,0:T(8,128)(2,1)}, u32[]{:S(2)}) copy-start(bf16[8,3,256,256]{3,2,1,0:T(8,128)(2,1)} %last_ref.3) | copy-start | bytes 9437188
  47.1 2.1 %collective-permute-start.7 = (bf16[4,2,9,32,128]{4,3,2,1,0:T(8,128)(2,1)S(1)}, bf16[4,2,9,32,128]{4,3,2,1,0:T(8,128)(2,1)S(1)}, u32[]{:S(2)}, u32[]{:S(2)}) collective-permute-start(bf16[4,2,9,32,128]{4,3,2,1,0:T(8,128)(2,1)S(1)} %get-tuple-element.71), channel_id=1, source_target_pairs={{0,1},{1,0},{2,3},{3,2},{4,5},{5,4},{6,7},{7,6},{8,9},{9,8},{10,11... | collective-permute-start | bytes 1769480 | tf_op jit(solution)/shard_map/ppermute | solution.py:235
  49.3 10.0 %collective-permute-start.8 = (bf16[4,2,9,32,128]{4,3,2,1,0:T(8,128)(2,1)S(1)}, bf16[4,2,9,32,128]{4,3,2,1,0:T(8,128)(2,1)S(1)}, u32[]{:S(2)}, u32[]{:S(2)}) collective-permute-start(bf16[4,2,9,32,128]{4,3,2,1,0:T(8,128)(2,1)S(1)} %shard_map.102), channel_id=1, source_target_pairs={{0,8},{1,3},{2,10},{3,1},{4,12},{5,7},{6,14},{7,5},{8,0},{9,11},{1... | collective-permute-start | bytes 1769480 | tf_op jit(solution)/shard_map/ppermute | solution.py:230
  51.4 7.9 %collective-permute-start.9 = (bf16[4,2,9,32,128]{4,3,2,1,0:T(8,128)(2,1)S(1)}, bf16[4,2,9,32,128]{4,3,2,1,0:T(8,128)(2,1)S(1)}, u32[]{:S(2)}, u32[]{:S(2)}) collective-permute-start(bf16[4,2,9,32,128]{4,3,2,1,0:T(8,128)(2,1)S(1)} %get-tuple-element.74), channel_id=1, source_target_pairs={{0,1},{1,0},{2,3},{3,2},{4,5},{5,4},{6,7},{7,6},{8,9},{9,8},{10,11... | collective-permute-start | bytes 1769480 | tf_op jit(solution)/shard_map/ppermute | solution.py:235
  51.4 25.6 %copy-start.7 = (s32[12]{0:T(128)S(1)}, s32[12]{0:T(128)}, u32[]{:S(2)}) copy-start(s32[12]{0:T(128)} %ranks_ref.5) | copy-start | bytes 148
  51.4 2.0 %collective-permute-start.10 = (bf16[1,32,256]{2,1,0:T(8,128)(2,1)S(1)}, bf16[1,32,256]{2,1,0:T(8,128)(2,1)S(1)}, u32[]{:S(2)}, u32[]{:S(2)}) collective-permute-start(bf16[1,32,256]{2,1,0:T(8,128)(2,1)S(1)} %copy-done.10), channel_id=1, source_target_pairs={{0,1},{1,0},{2,3},{3,2},{4,5},{5,4},{6,7},{7,6},{8,9},{9,8},{10,11... | collective-permute-start | bytes 49160 | tf_op jit(solution)/shard_map/ppermute | solution.py:235
  51.9 1.5 %collective-permute-start.11 = (bf16[1,32,256]{2,1,0:T(8,128)(2,1)S(1)}, bf16[1,32,256]{2,1,0:T(8,128)(2,1)S(1)}, u32[]{:S(2)}, u32[]{:S(2)}) collective-permute-start(bf16[1,32,256]{2,1,0:T(8,128)(2,1)S(1)} %collective-permute-done.1), channel_id=1, source_target_pairs={{0,1},{1,0},{2,3},{3,2},{4,5},{5,4},{6,7},{7,6},{8,9},{9,8},{10,11... | collective-permute-start | bytes 49160 | tf_op jit(solution)/shard_map/ppermute | solution.py:235
  53.6 23.4 %copy-start.2 = (bf16[8,96,256]{2,1,0:T(8,128)(2,1)S(1)}, bf16[8,96,256]{2,1,0:T(8,128)(2,1)}, u32[]{:S(2)}) copy-start(bf16[8,96,256]{2,1,0:T(8,128)(2,1)} %basis_ref.3) | copy-start | bytes 1179652
  53.6 23.4 %copy-start.3 = (bf16[8,96,96]{2,1,0:T(8,128)(2,1)S(1)}, bf16[8,96,96]{2,1,0:T(8,128)(2,1)}, u32[]{:S(2)}) copy-start(bf16[8,96,96]{2,1,0:T(8,128)(2,1)} %transfer_ref.3) | copy-start | bytes 442372
  59.5 6.8 %collective-permute-start.12 = (bf16[1,4,9,32,128]{4,3,2,1,0:T(8,128)(2,1)S(1)}, bf16[1,4,9,32,128]{4,3,2,1,0:T(8,128)(2,1)S(1)}, u32[]{:S(2)}, u32[]{:S(2)}) collective-permute-start(bf16[1,4,9,32,128]{4,3,2,1,0:T(8,128)(2,1)S(1)} %get-tuple-element.82), channel_id=1, source_target_pairs={{0,4},{1,9},{2,6},{3,11},{4,0},{5,13},{6,2},{7,15},{8,12},{9,1},{1... | collective-permute-start | bytes 884744 | tf_op jit(solution)/shard_map/ppermute | solution.py:230
  66.4 5.2 %collective-permute-start.13 = (bf16[1,2,9,32,128]{4,3,2,1,0:T(8,128)(2,1)S(1)}, bf16[1,2,9,32,128]{4,3,2,1,0:T(8,128)(2,1)S(1)}, u32[]{:S(2)}, u32[]{:S(2)}) collective-permute-start(bf16[1,2,9,32,128]{4,3,2,1,0:T(8,128)(2,1)S(1)} %get-tuple-element.84), channel_id=1, source_target_pairs={{0,2},{1,5},{2,0},{3,7},{4,6},{5,1},{6,4},{7,3},{8,10},{9,13},{10,... | collective-permute-start | bytes 442376 | tf_op jit(solution)/shard_map/ppermute | solution.py:230
  71.6 5.4 %collective-permute-start.14 = (bf16[1,9,32,128]{3,2,1,0:T(8,128)(2,1)S(1)}, bf16[1,9,32,128]{3,2,1,0:T(8,128)(2,1)S(1)}, u32[]{:S(2)}, u32[]{:S(2)}) collective-permute-start(bf16[1,9,32,128]{3,2,1,0:T(8,128)(2,1)S(1)} %get-tuple-element.86), channel_id=1, source_target_pairs={{0,16},{1,17},{2,18},{3,19},{4,20},{5,21},{6,22},{7,23},{8,24},{9,... | collective-permute-start | bytes 221192 | tf_op jit(solution)/shard_map/ppermute | solution.py:226
  79.6 5.3 %collective-permute-start.15 = (bf16[9,32,128]{2,1,0:T(8,128)(2,1)S(1)}, bf16[9,32,128]{2,1,0:T(8,128)(2,1)S(1)}, u32[]{:S(2)}, u32[]{:S(2)}) collective-permute-start(bf16[9,32,128]{2,1,0:T(8,128)(2,1)S(1)} %get-tuple-element.88.refs_0_), channel_id=1, source_target_pairs={{0,16},{1,17},{2,18},{3,19},{4,20},{5,21},{6,22},{7,23},{8,24},{9,... | collective-permute-start | bytes 221192 | tf_op jit(solution)/shard_map/ppermute | solution.py:226
  84.8 5.2 %collective-permute-start.16 = (bf16[2,9,32,128]{3,2,1,0:T(8,128)(2,1)S(1)}, bf16[2,9,32,128]{3,2,1,0:T(8,128)(2,1)S(1)}, u32[]{:S(2)}, u32[]{:S(2)}) collective-permute-start(bf16[2,9,32,128]{3,2,1,0:T(8,128)(2,1)S(1)} %shard_map.108.refs_0_), channel_id=1, source_target_pairs={{0,2},{1,5},{2,0},{3,7},{4,6},{5,1},{6,4},{7,3},{8,10},{9,13},{10,... | collective-permute-start | bytes 442376 | tf_op jit(solution)/shard_map/ppermute | solution.py:230
  90.1 6.8 %collective-permute-start.17 = (bf16[2,2,9,32,128]{4,3,2,1,0:T(8,128)(2,1)S(1)}, bf16[2,2,9,32,128]{4,3,2,1,0:T(8,128)(2,1)S(1)}, u32[]{:S(2)}, u32[]{:S(2)}) collective-permute-start(bf16[2,2,9,32,128]{4,3,2,1,0:T(8,128)(2,1)S(1)} %shard_map.109.refs_0_), channel_id=1, source_target_pairs={{0,4},{1,9},{2,6},{3,11},{4,0},{5,13},{6,2},{7,15},{8,12},{9,1},{1... | collective-permute-start | bytes 884744 | tf_op jit(solution)/shard_map/ppermute | solution.py:230
  96.9 3.6 %collective-permute-start.19 = (bf16[4,2,9,32,128]{4,3,2,1,0:T(8,128)(2,1)S(1)}, bf16[4,2,9,32,128]{4,3,2,1,0:T(8,128)(2,1)S(1)}, u32[]{:S(2)}, u32[]{:S(2)}) collective-permute-start(bf16[4,2,9,32,128]{4,3,2,1,0:T(8,128)(2,1)S(1)} %bitcast.17), channel_id=1, source_target_pairs={{0,1},{1,0},{2,3},{3,2},{4,5},{5,4},{6,7},{7,6},{8,9},{9,8},{10,11... | collective-permute-start | bytes 1769480 | tf_op jit(solution)/shard_map/ppermute | solution.py:235
  97.0 9.9 %collective-permute-start.18 = (bf16[4,2,9,32,128]{4,3,2,1,0:T(8,128)(2,1)S(1)}, bf16[4,2,9,32,128]{4,3,2,1,0:T(8,128)(2,1)S(1)}, u32[]{:S(2)}, u32[]{:S(2)}) collective-permute-start(bf16[4,2,9,32,128]{4,3,2,1,0:T(8,128)(2,1)S(1)} %bitcast.18), channel_id=1, source_target_pairs={{0,8},{1,3},{2,10},{3,1},{4,12},{5,7},{6,14},{7,5},{8,0},{9,11},{1... | collective-permute-start | bytes 1769480 | tf_op jit(solution)/shard_map/ppermute | solution.py:230
  99.0 0.9 copy-start.5
  106.9 5.8 %collective-permute-start.20 = (bf16[4,2,9,32,128]{4,3,2,1,0:T(8,128)(2,1)S(1)}, bf16[4,2,9,32,128]{4,3,2,1,0:T(8,128)(2,1)S(1)}, u32[]{:S(2)}, u32[]{:S(2)}) collective-permute-start(bf16[4,2,9,32,128]{4,3,2,1,0:T(8,128)(2,1)S(1)} %collective-permute-done.18.refs_1_), channel_id=1, source_target_pairs={{0,1},{1,0},{2,3},{3,2},{4,5},{5,4},{6,7},{7,6},{8,9},{9,8},{10,11... | collective-permute-start | bytes 1769480 | tf_op jit(solution)/shard_map/ppermute | solution.py:235
  106.9 5.8 %collective-permute-start.21 = (bf16[1,32,256]{2,1,0:T(8,128)(2,1)S(1)}, bf16[1,32,256]{2,1,0:T(8,128)(2,1)S(1)}, u32[]{:S(2)}, u32[]{:S(2)}) collective-permute-start(bf16[1,32,256]{2,1,0:T(8,128)(2,1)S(1)} %get-tuple-element.95), channel_id=1, source_target_pairs={{1,3},{3,5},{5,7},{7,9},{9,11},{11,13},{13,15},{15,17},{17,19},{19... | collective-permute-start | bytes 49160 | tf_op jit(solution)/shard_map/ppermute | solution.py:356
  118.1 2.1 %collective-permute-start.22 = (bf16[4,2,9,32,128]{4,3,2,1,0:T(8,128)(2,1)S(1)}, bf16[4,2,9,32,128]{4,3,2,1,0:T(8,128)(2,1)S(1)}, u32[]{:S(2)}, u32[]{:S(2)}) collective-permute-start(bf16[4,2,9,32,128]{4,3,2,1,0:T(8,128)(2,1)S(1)} %get-tuple-element.98), channel_id=1, source_target_pairs={{0,1},{1,0},{2,3},{3,2},{4,5},{5,4},{6,7},{7,6},{8,9},{9,8},{10,11... | collective-permute-start | bytes 1769480 | tf_op jit(solution)/shard_map/ppermute | solution.py:235
  120.3 10.5 %collective-permute-start.23 = (bf16[4,2,9,32,128]{4,3,2,1,0:T(8,128)(2,1)S(1)}, bf16[4,2,9,32,128]{4,3,2,1,0:T(8,128)(2,1)S(1)}, u32[]{:S(2)}, u32[]{:S(2)}) collective-permute-start(bf16[4,2,9,32,128]{4,3,2,1,0:T(8,128)(2,1)S(1)} %shard_map.113), channel_id=1, source_target_pairs={{0,8},{1,3},{2,10},{3,1},{4,12},{5,7},{6,14},{7,5},{8,0},{9,11},{1... | collective-permute-start | bytes 1769480 | tf_op jit(solution)/shard_map/ppermute | solution.py:230
  122.9 7.9 %collective-permute-start.24 = (bf16[4,2,9,32,128]{4,3,2,1,0:T(8,128)(2,1)S(1)}, bf16[4,2,9,32,128]{4,3,2,1,0:T(8,128)(2,1)S(1)}, u32[]{:S(2)}, u32[]{:S(2)}) collective-permute-start(bf16[4,2,9,32,128]{4,3,2,1,0:T(8,128)(2,1)S(1)} %get-tuple-element.101), channel_id=1, source_target_pairs={{0,1},{1,0},{2,3},{3,2},{4,5},{5,4},{6,7},{7,6},{8,9},{9,8},{10,11... | collective-permute-start | bytes 1769480 | tf_op jit(solution)/shard_map/ppermute | solution.py:235
  122.9 2.0 %collective-permute-start.25 = (bf16[1,32,256]{2,1,0:T(8,128)(2,1)S(1)}, bf16[1,32,256]{2,1,0:T(8,128)(2,1)S(1)}, u32[]{:S(2)}, u32[]{:S(2)}) collective-permute-start(bf16[1,32,256]{2,1,0:T(8,128)(2,1)S(1)} %get-tuple-element.102), channel_id=1, source_target_pairs={{0,1},{1,0},{2,3},{3,2},{4,5},{5,4},{6,7},{7,6},{8,9},{9,8},{10,11... | collective-permute-start | bytes 49160 | tf_op jit(solution)/shard_map/ppermute | solution.py:235
  123.4 1.5 %collective-permute-start.26 = (bf16[1,32,256]{2,1,0:T(8,128)(2,1)S(1)}, bf16[1,32,256]{2,1,0:T(8,128)(2,1)S(1)}, u32[]{:S(2)}, u32[]{:S(2)}) collective-permute-start(bf16[1,32,256]{2,1,0:T(8,128)(2,1)S(1)} %collective-permute-done.21), channel_id=1, source_target_pairs={{0,1},{1,0},{2,3},{3,2},{4,5},{5,4},{6,7},{7,6},{8,9},{9,8},{10,11... | collective-permute-start | bytes 49160 | tf_op jit(solution)/shard_map/ppermute | solution.py:235
  131.0 6.8 %collective-permute-start.27 = (bf16[1,4,9,32,128]{4,3,2,1,0:T(8,128)(2,1)S(1)}, bf16[1,4,9,32,128]{4,3,2,1,0:T(8,128)(2,1)S(1)}, u32[]{:S(2)}, u32[]{:S(2)}) collective-permute-start(bf16[1,4,9,32,128]{4,3,2,1,0:T(8,128)(2,1)S(1)} %get-tuple-element.109), channel_id=1, source_target_pairs={{0,4},{1,9},{2,6},{3,11},{4,0},{5,13},{6,2},{7,15},{8,12},{9,1},{1... | collective-permute-start | bytes 884744 | tf_op jit(solution)/shard_map/ppermute | solution.py:230
  137.8 5.3 %collective-permute-start.28 = (bf16[1,2,9,32,128]{4,3,2,1,0:T(8,128)(2,1)S(1)}, bf16[1,2,9,32,128]{4,3,2,1,0:T(8,128)(2,1)S(1)}, u32[]{:S(2)}, u32[]{:S(2)}) collective-permute-start(bf16[1,2,9,32,128]{4,3,2,1,0:T(8,128)(2,1)S(1)} %get-tuple-element.111), channel_id=1, source_target_pairs={{0,2},{1,5},{2,0},{3,7},{4,6},{5,1},{6,4},{7,3},{8,10},{9,13},{10,... | collective-permute-start | bytes 442376 | tf_op jit(solution)/shard_map/ppermute | solution.py:230
  143.2 5.3 %collective-permute-start.29 = (bf16[1,9,32,128]{3,2,1,0:T(8,128)(2,1)S(1)}, bf16[1,9,32,128]{3,2,1,0:T(8,128)(2,1)S(1)}, u32[]{:S(2)}, u32[]{:S(2)}) collective-permute-start(bf16[1,9,32,128]{3,2,1,0:T(8,128)(2,1)S(1)} %get-tuple-element.113), channel_id=1, source_target_pairs={{0,16},{1,17},{2,18},{3,19},{4,20},{5,21},{6,22},{7,23},{8,24},{9,... | collective-permute-start | bytes 221192 | tf_op jit(solution)/shard_map/ppermute | solution.py:226

commit v11 on v9

--- a/solution.py
+++ b/solution.py
@@ -154,6 +154,19 @@
 def add_kernel(keep_ref, swap_ref, *out_refs):
     for n, out_ref in enumerate(out_refs):
         out_ref[...] = (keep_ref[n].astype(F32) + swap_ref[n].astype(F32)).astype(out_ref.dtype)
+
+
+def middle_add_kernel(keep_ref, swap_ref, *refs, parts):
+    part_refs, (own_out, *out_refs) = refs[:parts], refs[parts:]
+    own_out[...] = keep_ref[0].astype(F32) + swap_ref[0].astype(F32)
+    for n, (part_ref, out_ref) in enumerate(zip(part_refs, out_refs)):
+        total = keep_ref[n + 1].astype(F32) + swap_ref[n + 1].astype(F32)
+        out_ref[...] = (total + part_ref[...].astype(F32)).astype(BF)
+
+
+def join_kernel(*refs):
+    for n, part_ref in enumerate(refs[:-1]):
+        refs[-1][n] = part_ref[...]
 
 
 def last_add_kernel(own_ref, *refs, parts):
@@ -313,12 +326,11 @@
         )
 
     own_shape = shape((far,) + tile_shape, F32)
+    join = adder(join_kernel, far, [part_shape])
     far_add = adder(add_kernel, 2, [part_shape] * 4)
-    near_add = adder(add_kernel, 2, [own_shape] + [part_shape] * 3)
+    middle_add = adder(functools.partial(middle_add_kernel, parts=3), 5, [own_shape] + [part_shape] * 3)
     last_add = adder(
-        functools.partial(last_add_kernel, parts=chips - 1),
-        chips,
-        [shape(tile_shape, F32)] + [tile_out] * (far - 1),
+        functools.partial(last_add_kernel, parts=4), 5, [shape(tile_shape, F32)] + [tile_out] * (far - 1)
     )
 
     def finish(with_coeffs):
@@ -333,18 +345,18 @@
     halo_pairs = [(d, d + cores) for d in range(1, devices - cores, cores)]
     halo_pairs += [(d, d - cores) for d in range(cores, devices, cores)]
 
-    long, short = order[0], order[1][1:]
-
     def apply_matrix(field_in, coeffs, inner, outer, coupling, with_coeffs):
-        away = [swap_far(coeffs, s) for s in range(1, far)]
+        (column,) = join(coeffs, *[swap_far(coeffs, s) for s in range(1, far)])
+        got = {0: column, x: swap(column, x), y: swap(column, y), z: swap(column, z)}
+        got, coupling = barrier((got, coupling))
+        corner = swap(column, x | y | z)
+        other = {chip: swap_cores(part) for chip, part in got.items()}
+        got |= {x | y: swap(got[x], y), y | z: swap(got[y], z), z | x: swap(got[z], x)}
         outer = lax.ppermute(outer, "clu", halo_pairs)
-        away, outer, coupling = barrier((away, outer, coupling))
-        column = jnp.stack([coeffs] + away)
-        got = {chip: swap(column, chip) for chip in long + short}
         near_sum = near(field_in, near_field)
-        got, near_sum = barrier((got, near_sum))
-        got[0] = column
-        other = {chip: swap_cores(got[chip]) for chip in got}
+        got, corner, outer, near_sum = barrier((got, corner, outer, near_sum))
+        got[x | y | z] = corner
+        other |= {chip: swap_cores(got[chip]) for chip in order[0]}
         keep_long, keep, send_long, send = couple(
             source_rows,
             target_rows,
@@ -352,13 +364,14 @@
             *[got[chip] for chip in range(chips)],
             *[other[chip] for chip in range(chips)],
         )
-        parts = far_add(keep_long, swap_cores(send_long))
-        own, *rest = near_add(keep, swap_cores(send))
-        parts = [swap(part, chip) for part, chip in zip([*parts, *rest], long + short)]
-        total, *away = last_add(own, *parts)
-        terms = [swap_far(part, s + 1) for s, part in enumerate(away)]
+        corner, xy, yz, zx = far_add(keep_long, swap_cores(send_long))
+        corner, xy, yz, zx, send = barrier((corner, xy, yz, zx, send))
         inner, outer = swap_cores(inner), swap_cores(outer)
         edges = edge(core_index, inner, outer, near_field, near_field)
+        to_x, to_y, to_z, swapped, edges = barrier((swap(xy, y), swap(yz, z), swap(zx, x), swap_cores(send), edges))
+        own, to_x, to_y, to_z = middle_add(keep, swapped, to_x, to_y, to_z)
+        total, *away = last_add(own, swap(to_x, x), swap(to_y, y), swap(to_z, z), swap(corner, x | y | z))
+        terms = [swap_far(part, s + 1) for s, part in enumerate(away)]
         return finish(with_coeffs)(ranks, core_index, near_sum, edges, basis, transfer, total, *terms)
 
     coupling, first_coeffs = barrier((coupling, first_coeffs))
@@ -368,6 +381,7 @@
         in_specs=[pl.BlockSpec(memory_space=pl.ANY)],
         out_specs=pl.BlockSpec(memory_space=pl.ANY),
         input_output_aliases={0: 0},
+        compiler_params=params(1),
     )(coupling)
     first, *second_args = apply_matrix(charges, first_coeffs, inner, outer, coupling, True)
     (second,) = apply_matrix(first, *second_args, coupling, False)

time: 157 us -> 135 us (0.86)
  waiting for transfers between devices: 58.6 us -> 48.5 us
  starting transfers between devices: 60.2 us -> 52.8 us
  local copies, waits for them, and re-layouts: 14.6 us -> 10.8 us
    ppermute x28, waiting for transfers between devices: 39.1 us -> 16.4 us  [swap(): lax.ppermute(part, 'clu', [(d, d ^ (turned if d % cores else direction) *...]
    ppermute x4, waiting for transfers between devices: 6.51 us -> 20.1 us  [swap_far(): lax.ppermute(part, 'clu', [(d, (d + shift * cube) % devices) for d in ran...]
    ppermute x28, starting transfers between devices: 42.8 us -> 36.7 us  [swap(): lax.ppermute(part, 'clu', [(d, d ^ (turned if d % cores else direction) *...]
    unnamed x42 -> x32, local copies, waits for them, and re-layouts: 9.78 us -> 6.02 us
    ppermute x2, waiting for transfers between devices: 5.48 us -> 2.09 us  [apply_matrix(): outer = lax.ppermute(outer, 'clu', halo_pairs)]
    ppermute x24, waiting for transfers between devices: 7.54 us -> 9.9 us  [swap_cores(): return lax.ppermute(part, 'clu', [(d, d ^ 1) for d in range(devices)])]
    ppermute x4, starting transfers between devices: 9.7 us -> 7.89 us  [swap_far(): lax.ppermute(part, 'clu', [(d, (d + shift * cube) % devices) for d in ran...]
  transfers between devices with their start and end apart: 58 -> 58, of which waited for: 31 -> 27; matrix products, arithmetic and copies ran while one was open for 4% -> 4% of each run, Pallas kernels for 1% -> 1%
where the time goes in v11:
time: 135 us
  starting transfers between devices  52.8 us (39%)
  waiting for transfers between devices  48.5 us (36%)
  Pallas kernels  21.7 us (16%)
  local copies, waits for them, and re-layouts  10.8 us (8%)
    ppermute x28, starting transfers between devices, swap(): lax.ppermute(part, 'clu', [(d, d ^ (turned if d % cores else direction) *...  36.7 us
    ppermute x4, waiting for transfers between devices, swap_far(): lax.ppermute(part, 'clu', [(d, (d + shift * cube) % devices) for d in ran...  20.1 us
    ppermute x28, waiting for transfers between devices, swap(): lax.ppermute(part, 'clu', [(d, d ^ (turned if d % cores else direction) *...  16.4 us
    pallas_call x2, Pallas kernels, apply_matrix(): couple(source_rows, target_rows, coupling, *[got[chip] for chip in range(...  11.5 us
    ppermute x24, waiting for transfers between devices, swap_cores(): return lax.ppermute(part, 'clu', [(d, d ^ 1) for d in range(devices)])  9.9 us
    ppermute x4, starting transfers between devices, swap_far(): lax.ppermute(part, 'clu', [(d, (d + shift * cube) % devices) for d in ran...  7.89 us
    unnamed x32, local copies, waits for them, and re-layouts  6.02 us
    ppermute x24, starting transfers between devices, swap_cores(): return lax.ppermute(part, 'clu', [(d, d ^ 1) for d in range(devices)])  5.57 us
  transfers between devices with their start and end apart: 58, of which 27 were waited for; matrix products, arithmetic and copies ran while one was open for 4% of the time, Pallas kernels for 1%

profile of v11, /device:TPU:0, one launch (start us, length us, event | category | flops | bytes accessed | tf_op | source)
XLA Modules:
  0.0 134.6 jit_solution(7300696127366195529)
XLA Ops:
  0.6 2.9 %shard_map.95 = (bf16[9,32,128]{2,1,0:T(8,128)(2,1)}, bf16[1,32,256]{2,1,0:T(8,128)(2,1)}, bf16[1,32,256]{2,1,0:T(8,128)(2,1)}) custom-call(s32[12]{0:T(128)} %ranks_ref.5, s32[1]{0:T(128)} %bitcast.core_ref, bf16[8,32,256]{2,1,0:T(8,128)(2,1)} %v_ref.1, bf16[8,96,256]{2,1,0:T(8,128)(2,1)} %basis_ref.3, bf16[8,96,96]{2,1,0:T(8,128)(2,1)} %transfer_ref.3), custom_call_target="tpu_custom_call" | custom-call | tf_op jit(solution)/shard_map/pallas_call | solution.py:264
  3.5 4.1 %collective-permute-start = (bf16[9,32,128]{2,1,0:T(8,128)(2,1)}, bf16[9,32,128]{2,1,0:T(8,128)(2,1)S(1)}, u32[]{:S(2)}, u32[]{:S(2)}) collective-permute-start(bf16[9,32,128]{2,1,0:T(8,128)(2,1)} %get-tuple-element.90.refs_0_), channel_id=1, source_target_pairs={{0,16},{1,17},{2,18},{3,19},{4,20},{5,21},{6,22},{7,23},{8,24},{9,... | collective-permute-start | bytes 221192 | tf_op jit(solution)/shard_map/ppermute | solution.py:233
  7.6 4.1 %collective-permute-done.refs_1_ = bf16[9,32,128]{2,1,0:T(8,128)(2,1)S(1)} collective-permute-done((bf16[9,32,128]{2,1,0:T(8,128)(2,1)}, bf16[9,32,128]{2,1,0:T(8,128)(2,1)S(1)}, u32[]{:S(2)}, u32[]{:S(2)}) %collective-permute-start) | collective-permute-done | bytes 73760 | tf_op jit(solution)/shard_map/ppermute | solution.py:233
  11.8 0.9 copy-done.10
  12.7 1.8 %collective-permute-start.1 = (bf16[2,9,32,128]{3,2,1,0:T(8,128)(2,1)S(1)}, bf16[2,9,32,128]{3,2,1,0:T(8,128)(2,1)}, u32[]{:S(2)}, u32[]{:S(2)}) collective-permute-start(bf16[2,9,32,128]{3,2,1,0:T(8,128)(2,1)S(1)} %shard_map.96.refs_0_), channel_id=1, source_target_pairs={{0,2},{1,5},{2,0},{3,7},{4,6},{5,1},{6,4},{7,3},{8,10},{9,13},{10,... | collective-permute-start | bytes 442376 | tf_op jit(solution)/shard_map/ppermute | solution.py:237
  14.4 1.5 %collective-permute-start.2 = (bf16[2,9,32,128]{3,2,1,0:T(8,128)(2,1)S(1)}, bf16[2,9,32,128]{3,2,1,0:T(8,128)(2,1)}, u32[]{:S(2)}, u32[]{:S(2)}) collective-permute-start(bf16[2,9,32,128]{3,2,1,0:T(8,128)(2,1)S(1)} %shard_map.96.refs_0_), channel_id=1, source_target_pairs={{0,4},{1,9},{2,6},{3,11},{4,0},{5,13},{6,2},{7,15},{8,12},{9,1},{1... | collective-permute-start | bytes 442376 | tf_op jit(solution)/shard_map/ppermute | solution.py:237
  16.0 0.6 collective-permute-start.3
  16.5 4.7 %copy.11.in_ref = bf16[128,96,96]{2,1,0:T(8,128)(2,1)} copy(bf16[128,96,96]{0,2,1:T(8,128)(2,1)} %param.12) | data formatting | bytes 4718592 | tf_op jit(solution)/shard_map/optimization_barrier | solution.py:377
  21.2 1.9 %copy-done.1 = bf16[128,96,96]{2,1,0:T(8,128)(2,1)S(1)} copy-done((bf16[128,96,96]{2,1,0:T(8,128)(2,1)S(1)}, bf16[128,96,96]{2,1,0:T(8,128)(2,1)}, u32[]{:S(2)}) %copy-start.1) | copy-done | bytes 2359320
  23.1 1.6 %copy-done.2 = bf16[128,96,96]{2,1,0:T(8,128)(2,1)} copy-done((bf16[128,96,96]{2,1,0:T(8,128)(2,1)}, bf16[128,96,96]{2,1,0:T(8,128)(2,1)S(1)}, u32[]{:S(2)}) %copy-start.2) | copy-done | bytes 2359320
  24.8 1.2 collective-permute-start.7
  26.0 1.8 %collective-permute-start.4 = (bf16[2,9,32,128]{3,2,1,0:T(8,128)(2,1)}, bf16[2,9,32,128]{3,2,1,0:T(8,128)(2,1)}, u32[]{:S(2)}, u32[]{:S(2)}) collective-permute-start(bf16[2,9,32,128]{3,2,1,0:T(8,128)(2,1)} %collective-permute-done.1.refs_1_), channel_id=1, source_target_pairs={{0,4},{1,9},{2,6},{3,11},{4,0},{5,13},{6,2},{7,15},{8,12},{9,1},{1... | collective-permute-start | bytes 442376 | tf_op jit(solution)/shard_map/ppermute | solution.py:237
  27.8 1.3 collective-permute-start.8
  29.1 2.7 %collective-permute-start.5 = (bf16[2,9,32,128]{3,2,1,0:T(8,128)(2,1)}, bf16[2,9,32,128]{3,2,1,0:T(8,128)(2,1)}, u32[]{:S(2)}, u32[]{:S(2)}) collective-permute-start(bf16[2,9,32,128]{3,2,1,0:T(8,128)(2,1)} %collective-permute-done.3.refs_4_), channel_id=1, source_target_pairs={{0,2},{1,5},{2,0},{3,7},{4,6},{5,1},{6,4},{7,3},{8,10},{9,13},{10,... | collective-permute-start | bytes 442376 | tf_op jit(solution)/shard_map/ppermute | solution.py:237
  31.8 0.9 collective-permute-start.6
  32.7 0.8 collective-permute-done.8
  33.5 0.7 copy-done.7
  34.8 0.6 shard_map.98.near_ref
  35.9 1.3 collective-permute-done.6.refs_6_
  37.2 0.5 collective-permute-start.14
  39.3 6.2 %shard_map.99 = (bf16[4,2,9,32,128]{4,3,2,1,0:T(8,128)(2,1)S(1)}, bf16[4,2,9,32,128]{4,3,2,1,0:T(8,128)(2,1)S(1)}, bf16[4,2,9,32,128]{4,3,2,1,0:T(8,128)(2,1)S(1)}, bf16[4,2,9,32,128]{4,3,2,1,0:T(8,128)(2,1)S(1)}) custom-call(s32[128]{0:T(128)S(1)} %get-tuple-element.176.source_ref, s32[128]{0:T(128)S(1)} %get-tuple-element.177.target_ref, ...), custom_call_target="tpu_custom_call" | custom-call | flops 75497472 | bytes 10485760 | tf_op jit(solution)/shard_map/pallas_call | solution.py:360
  45.9 1.7 %collective-permute-done.17.swap_ref = bf16[4,2,9,32,128]{4,3,2,1,0:T(8,128)(2,1)S(1)} collective-permute-done((bf16[4,2,9,32,128]{4,3,2,1,0:T(8,128)(2,1)S(1)}, bf16[4,2,9,32,128]{4,3,2,1,0:T(8,128)(2,1)S(1)}, u32[]{:S(2)}, u32[]{:S(2)}) %collective-permute-start.17) | collective-permute-done | bytes 589856 | tf_op jit(solution)/shard_map/ppermute | solution.py:242
  48.1 1.1 collective-permute-start.18
  49.2 0.6 collective-permute-start.19
  49.8 1.8 %collective-permute-start.20 = (bf16[2,9,32,128]{3,2,1,0:T(8,128)(2,1)S(1)}, bf16[2,9,32,128]{3,2,1,0:T(8,128)(2,1)S(1)}, u32[]{:S(2)}, u32[]{:S(2)}) collective-permute-start(bf16[2,9,32,128]{3,2,1,0:T(8,128)(2,1)S(1)} %get-tuple-element.116), channel_id=1, source_target_pairs={{0,2},{1,5},{2,0},{3,7},{4,6},{5,1},{6,4},{7,3},{8,10},{9,13},{10,... | collective-permute-start | bytes 442376 | tf_op jit(solution)/shard_map/ppermute | solution.py:237
  51.7 1.2 collective-permute-done.22.inner_ref
  53.0 1.0 collective-permute-done.23.outer_ref
  54.2 1.5 %collective-permute-start.27 = (bf16[2,9,32,128]{3,2,1,0:T(8,128)(2,1)S(1)}, bf16[2,9,32,128]{3,2,1,0:T(8,128)(2,1)S(1)}, u32[]{:S(2)}, u32[]{:S(2)}) collective-permute-start(bf16[2,9,32,128]{3,2,1,0:T(8,128)(2,1)S(1)} %get-tuple-element.130), channel_id=1, source_target_pairs={{0,14},{1,15},{2,12},{3,13},{4,10},{5,11},{6,8},{7,9},{8,6},{9,7},... | collective-permute-start | bytes 442376 | tf_op jit(solution)/shard_map/ppermute | solution.py:237
  55.9 1.1 collective-permute-start.24
  57.0 1.9 %collective-permute-start.25 = (bf16[2,9,32,128]{3,2,1,0:T(8,128)(2,1)S(1)}, bf16[2,9,32,128]{3,2,1,0:T(8,128)(2,1)S(1)}, u32[]{:S(2)}, u32[]{:S(2)}) collective-permute-start(bf16[2,9,32,128]{3,2,1,0:T(8,128)(2,1)S(1)} %get-tuple-element.128), channel_id=1, source_target_pairs={{0,4},{1,9},{2,6},{3,11},{4,0},{5,13},{6,2},{7,15},{8,12},{9,1},{1... | collective-permute-start | bytes 442376 | tf_op jit(solution)/shard_map/ppermute | solution.py:237
  58.9 0.5 collective-permute-start.26
  59.4 3.3 %collective-permute-done.27.refs_3_ = bf16[2,9,32,128]{3,2,1,0:T(8,128)(2,1)S(1)} collective-permute-done((bf16[2,9,32,128]{3,2,1,0:T(8,128)(2,1)S(1)}, bf16[2,9,32,128]{3,2,1,0:T(8,128)(2,1)S(1)}, u32[]{:S(2)}, u32[]{:S(2)}) %collective-permute-start.27) | collective-permute-done | bytes 147488 | tf_op jit(solution)/shard_map/ppermute | solution.py:237
  62.7 2.3 %collective-permute-done.24.refs_0_ = bf16[2,9,32,128]{3,2,1,0:T(8,128)(2,1)S(1)} collective-permute-done((bf16[2,9,32,128]{3,2,1,0:T(8,128)(2,1)S(1)}, bf16[2,9,32,128]{3,2,1,0:T(8,128)(2,1)S(1)}, u32[]{:S(2)}, u32[]{:S(2)}) %collective-permute-start.24) | collective-permute-done | bytes 147488 | tf_op jit(solution)/shard_map/ppermute | solution.py:237
  65.1 1.9 %collective-permute-start.28 = (bf16[9,32,128]{2,1,0:T(8,128)(2,1)S(1)}, bf16[9,32,128]{2,1,0:T(8,128)(2,1)S(1)}, u32[]{:S(2)}, u32[]{:S(2)}) collective-permute-start(bf16[9,32,128]{2,1,0:T(8,128)(2,1)S(1)} %get-tuple-element.132), channel_id=1, source_target_pairs={{0,16},{1,17},{2,18},{3,19},{4,20},{5,21},{6,22},{7,23},{8,24},{9,... | collective-permute-start | bytes 221192 | tf_op jit(solution)/shard_map/ppermute | solution.py:233
  67.0 4.9 %collective-permute-done.28.rest_0_ = bf16[9,32,128]{2,1,0:T(8,128)(2,1)S(1)} collective-permute-done((bf16[9,32,128]{2,1,0:T(8,128)(2,1)S(1)}, bf16[9,32,128]{2,1,0:T(8,128)(2,1)S(1)}, u32[]{:S(2)}, u32[]{:S(2)}) %collective-permute-start.28) | collective-permute-done | bytes 73760 | tf_op jit(solution)/shard_map/ppermute | solution.py:233
  72.0 2.5 %shard_map.104 = (bf16[8,32,256]{2,1,0:T(8,128)(2,1)}, bf16[9,32,128]{2,1,0:T(8,128)(2,1)S(1)}, bf16[1,32,256]{2,1,0:T(8,128)(2,1)S(1)}, bf16[1,32,256]{2,1,0:T(8,128)(2,1)S(1)}) custom-call(s32[12]{0:T(128)S(1)} %copy-done.11, s32[1]{0:T(128)} %bitcast.core_ref, f32[8,32,256]{2,1,0:T(8,128)S(1)} %shard_map.98.near_ref, ...), custom_call_target="tpu_custom_call" | custom-call | tf_op jit(solution)/shard_map/pallas_call | solution.py:375
  74.9 6.2 %collective-permute-done.29.refs_1_ = bf16[9,32,128]{2,1,0:T(8,128)(2,1)S(1)} collective-permute-done((bf16[9,32,128]{2,1,0:T(8,128)(2,1)S(1)}, bf16[9,32,128]{2,1,0:T(8,128)(2,1)S(1)}, u32[]{:S(2)}, u32[]{:S(2)}) %collective-permute-start.29) | collective-permute-done | bytes 73760 | tf_op jit(solution)/shard_map/ppermute | solution.py:233
  81.2 0.8 collective-permute-start.31
  81.9 4.2 %collective-permute-start.36 = (bf16[2,9,32,128]{3,2,1,0:T(8,128)(2,1)S(1)}, bf16[2,9,32,128]{3,2,1,0:T(8,128)(2,1)S(1)}, u32[]{:S(2)}, u32[]{:S(2)}) collective-permute-start(bf16[2,9,32,128]{3,2,1,0:T(8,128)(2,1)S(1)} %shard_map.105.refs_0_), channel_id=1, source_target_pairs={{0,14},{1,15},{2,12},{3,13},{4,10},{5,11},{6,8},{7,9},{8,6},{9,7},... | collective-permute-start | bytes 442376 | tf_op jit(solution)/shard_map/ppermute | solution.py:237
  86.1 2.6 %collective-permute-done.30.refs_1_ = bf16[2,9,32,128]{3,2,1,0:T(8,128)(2,1)S(1)} collective-permute-done((bf16[2,9,32,128]{3,2,1,0:T(8,128)(2,1)S(1)}, bf16[2,9,32,128]{3,2,1,0:T(8,128)(2,1)S(1)}, u32[]{:S(2)}, u32[]{:S(2)}) %collective-permute-start.30) | collective-permute-done | bytes 147488 | tf_op jit(solution)/shard_map/ppermute | solution.py:237
  88.7 1.3 %collective-permute-start.33 = (bf16[2,9,32,128]{3,2,1,0:T(8,128)(2,1)S(1)}, bf16[2,9,32,128]{3,2,1,0:T(8,128)(2,1)S(1)}, u32[]{:S(2)}, u32[]{:S(2)}) collective-permute-start(bf16[2,9,32,128]{3,2,1,0:T(8,128)(2,1)S(1)} %collective-permute-done.30.refs_1_), channel_id=1, source_target_pairs={{0,4},{1,9},{2,6},{3,11},{4,0},{5,13},{6,2},{7,15},{8,12},{9,1},{1... | collective-permute-start | bytes 442376 | tf_op jit(solution)/shard_map/ppermute | solution.py:237
  90.0 1.3 collective-permute-start.37
  91.3 2.7 %collective-permute-start.34 = (bf16[2,9,32,128]{3,2,1,0:T(8,128)(2,1)S(1)}, bf16[2,9,32,128]{3,2,1,0:T(8,128)(2,1)S(1)}, u32[]{:S(2)}, u32[]{:S(2)}) collective-permute-start(bf16[2,9,32,128]{3,2,1,0:T(8,128)(2,1)S(1)} %collective-permute-done.32.refs_4_), channel_id=1, source_target_pairs={{0,2},{1,5},{2,0},{3,7},{4,6},{5,1},{6,4},{7,3},{8,10},{9,13},{10,... | collective-permute-start | bytes 442376 | tf_op jit(solution)/shard_map/ppermute | solution.py:237
  94.0 0.5 collective-permute-start.35
  94.5 1.3 collective-permute-done.37
  96.4 0.9 copy-done.9
  97.3 0.6 shard_map.106.near_ref
  98.4 0.7 collective-permute-done.35.refs_6_
  101.2 5.3 %shard_map.107 = (bf16[4,2,9,32,128]{4,3,2,1,0:T(8,128)(2,1)S(1)}, bf16[4,2,9,32,128]{4,3,2,1,0:T(8,128)(2,1)S(1)}, bf16[4,2,9,32,128]{4,3,2,1,0:T(8,128)(2,1)S(1)}, bf16[4,2,9,32,128]{4,3,2,1,0:T(8,128)(2,1)S(1)}) custom-call(s32[128]{0:T(128)S(1)} %get-tuple-element.176.source_ref, s32[128]{0:T(128)S(1)} %get-tuple-element.177.target_ref, ...), custom_call_target="tpu_custom_call" | custom-call | flops 75497472 | bytes 10485760 | tf_op jit(solution)/shard_map/pallas_call | solution.py:360
  107.0 1.7 %collective-permute-done.46.swap_ref = bf16[4,2,9,32,128]{4,3,2,1,0:T(8,128)(2,1)S(1)} collective-permute-done((bf16[4,2,9,32,128]{4,3,2,1,0:T(8,128)(2,1)S(1)}, bf16[4,2,9,32,128]{4,3,2,1,0:T(8,128)(2,1)S(1)}, u32[]{:S(2)}, u32[]{:S(2)}) %collective-permute-start.46) | collective-permute-done | bytes 589856 | tf_op jit(solution)/shard_map/ppermute | solution.py:242
  109.2 0.7 collective-permute-start.47
  109.9 0.8 collective-permute-start.48
  110.7 1.6 %collective-permute-start.49 = (bf16[2,9,32,128]{3,2,1,0:T(8,128)(2,1)S(1)}, bf16[2,9,32,128]{3,2,1,0:T(8,128)(2,1)S(1)}, u32[]{:S(2)}, u32[]{:S(2)}) collective-permute-start(bf16[2,9,32,128]{3,2,1,0:T(8,128)(2,1)S(1)} %get-tuple-element.159), channel_id=1, source_target_pairs={{0,2},{1,5},{2,0},{3,7},{4,6},{5,1},{6,4},{7,3},{8,10},{9,13},{10,... | collective-permute-start | bytes 442376 | tf_op jit(solution)/shard_map/ppermute | solution.py:237
  112.3 1.2 collective-permute-done.51.inner_ref
  113.6 1.0 collective-permute-done.52.outer_ref
  114.8 1.8 %collective-permute-start.56 = (bf16[2,9,32,128]{3,2,1,0:T(8,128)(2,1)S(1)}, bf16[2,9,32,128]{3,2,1,0:T(8,128)(2,1)S(1)}, u32[]{:S(2)}, u32[]{:S(2)}) collective-permute-start(bf16[2,9,32,128]{3,2,1,0:T(8,128)(2,1)S(1)} %get-tuple-element.173), channel_id=1, source_target_pairs={{0,14},{1,15},{2,12},{3,13},{4,10},{5,11},{6,8},{7,9},{8,6},{9,7},... | collective-permute-start | bytes 442376 | tf_op jit(solution)/shard_map/ppermute | solution.py:237
  116.9 0.8 collective-permute-start.53
  117.7 1.8 %collective-permute-start.54 = (bf16[2,9,32,128]{3,2,1,0:T(8,128)(2,1)S(1)}, bf16[2,9,32,128]{3,2,1,0:T(8,128)(2,1)S(1)}, u32[]{:S(2)}, u32[]{:S(2)}) collective-permute-start(bf16[2,9,32,128]{3,2,1,0:T(8,128)(2,1)S(1)} %get-tuple-element.171), channel_id=1, source_target_pairs={{0,4},{1,9},{2,6},{3,11},{4,0},{5,13},{6,2},{7,15},{8,12},{9,1},{1... | collective-permute-start | bytes 442376 | tf_op jit(solution)/shard_map/ppermute | solution.py:237
  119.5 0.5 collective-permute-start.55
  120.1 3.2 %collective-permute-done.56.refs_3_ = bf16[2,9,32,128]{3,2,1,0:T(8,128)(2,1)S(1)} collective-permute-done((bf16[2,9,32,128]{3,2,1,0:T(8,128)(2,1)S(1)}, bf16[2,9,32,128]{3,2,1,0:T(8,128)(2,1)S(1)}, u32[]{:S(2)}, u32[]{:S(2)}) %collective-permute-start.56) | collective-permute-done | bytes 147488 | tf_op jit(solution)/shard_map/ppermute | solution.py:237
  123.3 2.4 %collective-permute-done.53.refs_0_ = bf16[2,9,32,128]{3,2,1,0:T(8,128)(2,1)S(1)} collective-permute-done((bf16[2,9,32,128]{3,2,1,0:T(8,128)(2,1)S(1)}, bf16[2,9,32,128]{3,2,1,0:T(8,128)(2,1)S(1)}, u32[]{:S(2)}, u32[]{:S(2)}) %collective-permute-start.53) | collective-permute-done | bytes 147488 | tf_op jit(solution)/shard_map/ppermute | solution.py:237
  125.8 1.5 %collective-permute-start.57 = (bf16[9,32,128]{2,1,0:T(8,128)(2,1)S(1)}, bf16[9,32,128]{2,1,0:T(8,128)(2,1)S(1)}, u32[]{:S(2)}, u32[]{:S(2)}) collective-permute-start(bf16[9,32,128]{2,1,0:T(8,128)(2,1)S(1)} %get-tuple-element.175), channel_id=1, source_target_pairs={{0,16},{1,17},{2,18},{3,19},{4,20},{5,21},{6,22},{7,23},{8,24},{9,... | collective-permute-start | bytes 221192 | tf_op jit(solution)/shard_map/ppermute | solution.py:233
  127.3 4.9 %collective-permute-done.57.rest_0_ = bf16[9,32,128]{2,1,0:T(8,128)(2,1)S(1)} collective-permute-done((bf16[9,32,128]{2,1,0:T(8,128)(2,1)S(1)}, bf16[9,32,128]{2,1,0:T(8,128)(2,1)S(1)}, u32[]{:S(2)}, u32[]{:S(2)}) %collective-permute-start.57) | collective-permute-done | bytes 73760 | tf_op jit(solution)/shard_map/ppermute | solution.py:233
  132.2 2.5 %shard_map.112 = bf16[8,32,256]{2,1,0:T(8,128)(2,1)} custom-call(s32[12]{0:T(128)S(1)} %copy-done.11, s32[1]{0:T(128)} %bitcast.core_ref, f32[8,32,256]{2,1,0:T(8,128)S(1)} %shard_map.106.near_ref, f32[2,32,256]{2,1,0:T(8,128)S(1)} %shard_map.109.edge_ref, bf16[8,96,256]{2,1,0:T(8,128)(2,1)S(1)} %copy-done.4, bf16[8,96,96]{2,1,0:T(8,128)(2,1)S(1)} %copy-done.5, ...), custom_call_target="tpu_custom_call" | custom-call | tf_op jit(solution)/shard_map/pallas_call | solution.py:375
  (104 shorter events, 9.4 us)
Async XLA Ops:
  3.5 8.2 %collective-permute-start = (bf16[9,32,128]{2,1,0:T(8,128)(2,1)}, bf16[9,32,128]{2,1,0:T(8,128)(2,1)S(1)}, u32[]{:S(2)}, u32[]{:S(2)}) collective-permute-start(bf16[9,32,128]{2,1,0:T(8,128)(2,1)} %get-tuple-element.90.refs_0_), channel_id=1, source_target_pairs={{0,16},{1,17},{2,18},{3,19},{4,20},{5,21},{6,22},{7,23},{8,24},{9,... | collective-permute-start | bytes 221192 | tf_op jit(solution)/shard_map/ppermute | solution.py:233
  12.7 13.3 %collective-permute-start.1 = (bf16[2,9,32,128]{3,2,1,0:T(8,128)(2,1)S(1)}, bf16[2,9,32,128]{3,2,1,0:T(8,128)(2,1)}, u32[]{:S(2)}, u32[]{:S(2)}) collective-permute-start(bf16[2,9,32,128]{3,2,1,0:T(8,128)(2,1)S(1)} %shard_map.96.refs_0_), channel_id=1, source_target_pairs={{0,2},{1,5},{2,0},{3,7},{4,6},{5,1},{6,4},{7,3},{8,10},{9,13},{10,... | collective-permute-start | bytes 442376 | tf_op jit(solution)/shard_map/ppermute | solution.py:237
  14.4 11.5 %collective-permute-start.2 = (bf16[2,9,32,128]{3,2,1,0:T(8,128)(2,1)S(1)}, bf16[2,9,32,128]{3,2,1,0:T(8,128)(2,1)}, u32[]{:S(2)}, u32[]{:S(2)}) collective-permute-start(bf16[2,9,32,128]{3,2,1,0:T(8,128)(2,1)S(1)} %shard_map.96.refs_0_), channel_id=1, source_target_pairs={{0,4},{1,9},{2,6},{3,11},{4,0},{5,13},{6,2},{7,15},{8,12},{9,1},{1... | collective-permute-start | bytes 442376 | tf_op jit(solution)/shard_map/ppermute | solution.py:237
  16.0 10.0 %collective-permute-start.3 = (bf16[2,9,32,128]{3,2,1,0:T(8,128)(2,1)S(1)}, bf16[2,9,32,128]{3,2,1,0:T(8,128)(2,1)}, u32[]{:S(2)}, u32[]{:S(2)}) collective-permute-start(bf16[2,9,32,128]{3,2,1,0:T(8,128)(2,1)S(1)} %shard_map.96.refs_0_), channel_id=1, source_target_pairs={{0,8},{1,3},{2,10},{3,1},{4,12},{5,7},{6,14},{7,5},{8,0},{9,11},{1... | collective-permute-start | bytes 442376 | tf_op jit(solution)/shard_map/ppermute | solution.py:237
  24.8 13.5 %copy-start.12 = (s32[128]{0:T(128)S(1)}, s32[128]{0:T(128)}, u32[]{:S(2)}) copy-start(s32[128]{0:T(128)} %param.14) | copy-start | bytes 1540
  24.8 13.5 %copy-start.13 = (s32[128]{0:T(128)S(1)}, s32[128]{0:T(128)}, u32[]{:S(2)}) copy-start(s32[128]{0:T(128)} %param.15) | copy-start | bytes 1540
  24.8 8.8 %collective-permute-start.7 = (bf16[2,9,32,128]{3,2,1,0:T(8,128)(2,1)S(1)}, bf16[2,9,32,128]{3,2,1,0:T(8,128)(2,1)S(1)}, u32[]{:S(2)}, u32[]{:S(2)}) collective-permute-start(bf16[2,9,32,128]{3,2,1,0:T(8,128)(2,1)S(1)} %shard_map.96.refs_0_), channel_id=1, source_target_pairs={{0,14},{1,15},{2,12},{3,13},{4,10},{5,11},{6,8},{7,9},{8,6},{9,7},... | collective-permute-start | bytes 442376 | tf_op jit(solution)/shard_map/ppermute | solution.py:237
  26.0 8.8 %collective-permute-start.4 = (bf16[2,9,32,128]{3,2,1,0:T(8,128)(2,1)}, bf16[2,9,32,128]{3,2,1,0:T(8,128)(2,1)}, u32[]{:S(2)}, u32[]{:S(2)}) collective-permute-start(bf16[2,9,32,128]{3,2,1,0:T(8,128)(2,1)} %collective-permute-done.1.refs_1_), channel_id=1, source_target_pairs={{0,4},{1,9},{2,6},{3,11},{4,0},{5,13},{6,2},{7,15},{8,12},{9,1},{1... | collective-permute-start | bytes 442376 | tf_op jit(solution)/shard_map/ppermute | solution.py:237
  27.8 5.8 %collective-permute-start.8 = (bf16[1,32,256]{2,1,0:T(8,128)(2,1)S(1)}, bf16[1,32,256]{2,1,0:T(8,128)(2,1)S(1)}, u32[]{:S(2)}, u32[]{:S(2)}) collective-permute-start(bf16[1,32,256]{2,1,0:T(8,128)(2,1)S(1)} %copy-done.15), channel_id=1, source_target_pairs={{1,3},{3,5},{5,7},{7,9},{9,11},{11,13},{13,15},{15,17},{17,19},{19... | collective-permute-start | bytes 49160 | tf_op jit(solution)/shard_map/ppermute | solution.py:355
  29.1 6.8 %collective-permute-start.5 = (bf16[2,9,32,128]{3,2,1,0:T(8,128)(2,1)}, bf16[2,9,32,128]{3,2,1,0:T(8,128)(2,1)}, u32[]{:S(2)}, u32[]{:S(2)}) collective-permute-start(bf16[2,9,32,128]{3,2,1,0:T(8,128)(2,1)} %collective-permute-done.3.refs_4_), channel_id=1, source_target_pairs={{0,2},{1,5},{2,0},{3,7},{4,6},{5,1},{6,4},{7,3},{8,10},{9,13},{10,... | collective-permute-start | bytes 442376 | tf_op jit(solution)/shard_map/ppermute | solution.py:237
  31.8 5.5 %collective-permute-start.6 = (bf16[2,9,32,128]{3,2,1,0:T(8,128)(2,1)}, bf16[2,9,32,128]{3,2,1,0:T(8,128)(2,1)}, u32[]{:S(2)}, u32[]{:S(2)}) collective-permute-start(bf16[2,9,32,128]{3,2,1,0:T(8,128)(2,1)} %collective-permute-done.2.refs_2_), channel_id=1, source_target_pairs={{0,8},{1,3},{2,10},{3,1},{4,12},{5,7},{6,14},{7,5},{8,0},{9,11},{1... | collective-permute-start | bytes 442376 | tf_op jit(solution)/shard_map/ppermute | solution.py:237
  33.5 3.7 %collective-permute-start.9 = (bf16[2,9,32,128]{3,2,1,0:T(8,128)(2,1)S(1)}, bf16[2,9,32,128]{3,2,1,0:T(8,128)(2,1)}, u32[]{:S(2)}, u32[]{:S(2)}) collective-permute-start(bf16[2,9,32,128]{3,2,1,0:T(8,128)(2,1)S(1)} %shard_map.96.refs_0_), channel_id=1, source_target_pairs={{0,1},{1,0},{2,3},{3,2},{4,5},{5,4},{6,7},{7,6},{8,9},{9,8},{10,11... | collective-permute-start | bytes 442376 | tf_op jit(solution)/shard_map/ppermute | solution.py:242
  34.2 3.5 %collective-permute-start.10 = (bf16[2,9,32,128]{3,2,1,0:T(8,128)(2,1)}, bf16[2,9,32,128]{3,2,1,0:T(8,128)(2,1)}, u32[]{:S(2)}, u32[]{:S(2)}) collective-permute-start(bf16[2,9,32,128]{3,2,1,0:T(8,128)(2,1)} %collective-permute-done.1.refs_1_), channel_id=1, source_target_pairs={{0,1},{1,0},{2,3},{3,2},{4,5},{5,4},{6,7},{7,6},{8,9},{9,8},{10,11... | collective-permute-start | bytes 442376 | tf_op jit(solution)/shard_map/ppermute | solution.py:242
  34.7 3.1 %collective-permute-start.11 = (bf16[2,9,32,128]{3,2,1,0:T(8,128)(2,1)}, bf16[2,9,32,128]{3,2,1,0:T(8,128)(2,1)}, u32[]{:S(2)}, u32[]{:S(2)}) collective-permute-start(bf16[2,9,32,128]{3,2,1,0:T(8,128)(2,1)} %collective-permute-done.2.refs_2_), channel_id=1, source_target_pairs={{0,1},{1,0},{2,3},{3,2},{4,5},{5,4},{6,7},{7,6},{8,9},{9,8},{10,11... | collective-permute-start | bytes 442376 | tf_op jit(solution)/shard_map/ppermute | solution.py:242
  35.8 2.5 %collective-permute-start.13 = (bf16[2,9,32,128]{3,2,1,0:T(8,128)(2,1)}, bf16[2,9,32,128]{3,2,1,0:T(8,128)(2,1)S(1)}, u32[]{:S(2)}, u32[]{:S(2)}) collective-permute-start(bf16[2,9,32,128]{3,2,1,0:T(8,128)(2,1)} %collective-permute-done.3.refs_4_), channel_id=1, source_target_pairs={{0,1},{1,0},{2,3},{3,2},{4,5},{5,4},{6,7},{7,6},{8,9},{9,8},{10,11... | collective-permute-start | bytes 442376 | tf_op jit(solution)/shard_map/ppermute | solution.py:242
  37.2 1.6 %collective-permute-start.12 = (bf16[2,9,32,128]{3,2,1,0:T(8,128)(2,1)}, bf16[2,9,32,128]{3,2,1,0:T(8,128)(2,1)S(1)}, u32[]{:S(2)}, u32[]{:S(2)}) collective-permute-start(bf16[2,9,32,128]{3,2,1,0:T(8,128)(2,1)} %collective-permute-done.4.refs_3_), channel_id=1, source_target_pairs={{0,1},{1,0},{2,3},{3,2},{4,5},{5,4},{6,7},{7,6},{8,9},{9,8},{10,11... | collective-permute-start | bytes 442376 | tf_op jit(solution)/shard_map/ppermute | solution.py:242
  37.2 1.8 %collective-permute-start.14 = (bf16[2,9,32,128]{3,2,1,0:T(8,128)(2,1)}, bf16[2,9,32,128]{3,2,1,0:T(8,128)(2,1)S(1)}, u32[]{:S(2)}, u32[]{:S(2)}) collective-permute-start(bf16[2,9,32,128]{3,2,1,0:T(8,128)(2,1)} %collective-permute-done.5.refs_5_), channel_id=1, source_target_pairs={{0,1},{1,0},{2,3},{3,2},{4,5},{5,4},{6,7},{7,6},{8,9},{9,8},{10,11... | collective-permute-start | bytes 442376 | tf_op jit(solution)/shard_map/ppermute | solution.py:242
  37.7 1.6 %collective-permute-start.15 = (bf16[2,9,32,128]{3,2,1,0:T(8,128)(2,1)}, bf16[2,9,32,128]{3,2,1,0:T(8,128)(2,1)S(1)}, u32[]{:S(2)}, u32[]{:S(2)}) collective-permute-start(bf16[2,9,32,128]{3,2,1,0:T(8,128)(2,1)} %collective-permute-done.6.refs_6_), channel_id=1, source_target_pairs={{0,1},{1,0},{2,3},{3,2},{4,5},{5,4},{6,7},{7,6},{8,9},{9,8},{10,11... | collective-permute-start | bytes 442376 | tf_op jit(solution)/shard_map/ppermute | solution.py:242
  37.8 1.5 %collective-permute-start.16 = (bf16[2,9,32,128]{3,2,1,0:T(8,128)(2,1)S(1)}, bf16[2,9,32,128]{3,2,1,0:T(8,128)(2,1)S(1)}, u32[]{:S(2)}, u32[]{:S(2)}) collective-permute-start(bf16[2,9,32,128]{3,2,1,0:T(8,128)(2,1)S(1)} %copy-done.8), channel_id=1, source_target_pairs={{0,1},{1,0},{2,3},{3,2},{4,5},{5,4},{6,7},{7,6},{8,9},{9,8},{10,11... | collective-permute-start | bytes 442376 | tf_op jit(solution)/shard_map/ppermute | solution.py:242
  39.3 12.3 %copy-start.14 = (bf16[1,32,256]{2,1,0:T(8,128)(2,1)S(1)}, bf16[1,32,256]{2,1,0:T(8,128)(2,1)}, u32[]{:S(2)}) copy-start(bf16[1,32,256]{2,1,0:T(8,128)(2,1)} %get-tuple-element.118) | copy-start | bytes 49156
  45.5 2.1 %collective-permute-start.17 = (bf16[4,2,9,32,128]{4,3,2,1,0:T(8,128)(2,1)S(1)}, bf16[4,2,9,32,128]{4,3,2,1,0:T(8,128)(2,1)S(1)}, u32[]{:S(2)}, u32[]{:S(2)}) collective-permute-start(bf16[4,2,9,32,128]{4,3,2,1,0:T(8,128)(2,1)S(1)} %get-tuple-element.108), channel_id=1, source_target_pairs={{0,1},{1,0},{2,3},{3,2},{4,5},{5,4},{6,7},{7,6},{8,9},{9,8},{10,11... | collective-permute-start | bytes 1769480 | tf_op jit(solution)/shard_map/ppermute | solution.py:242
  47.7 7.9 %collective-permute-start.21 = (bf16[4,2,9,32,128]{4,3,2,1,0:T(8,128)(2,1)S(1)}, bf16[4,2,9,32,128]{4,3,2,1,0:T(8,128)(2,1)S(1)}, u32[]{:S(2)}, u32[]{:S(2)}) collective-permute-start(bf16[4,2,9,32,128]{4,3,2,1,0:T(8,128)(2,1)S(1)} %get-tuple-element.117), channel_id=1, source_target_pairs={{0,1},{1,0},{2,3},{3,2},{4,5},{5,4},{6,7},{7,6},{8,9},{9,8},{10,11... | collective-permute-start | bytes 1769480 | tf_op jit(solution)/shard_map/ppermute | solution.py:242
  48.1 7.6 %collective-permute-start.18 = (bf16[2,9,32,128]{3,2,1,0:T(8,128)(2,1)S(1)}, bf16[2,9,32,128]{3,2,1,0:T(8,128)(2,1)S(1)}, u32[]{:S(2)}, u32[]{:S(2)}) collective-permute-start(bf16[2,9,32,128]{3,2,1,0:T(8,128)(2,1)S(1)} %get-tuple-element.114), channel_id=1, source_target_pairs={{0,4},{1,9},{2,6},{3,11},{4,0},{5,13},{6,2},{7,15},{8,12},{9,1},{1... | collective-permute-start | bytes 442376 | tf_op jit(solution)/shard_map/ppermute | solution.py:237
  49.2 6.4 %collective-permute-start.19 = (bf16[2,9,32,128]{3,2,1,0:T(8,128)(2,1)S(1)}, bf16[2,9,32,128]{3,2,1,0:T(8,128)(2,1)S(1)}, u32[]{:S(2)}, u32[]{:S(2)}) collective-permute-start(bf16[2,9,32,128]{3,2,1,0:T(8,128)(2,1)S(1)} %get-tuple-element.115), channel_id=1, source_target_pairs={{0,8},{1,3},{2,10},{3,1},{4,12},{5,7},{6,14},{7,5},{8,0},{9,11},{1... | collective-permute-start | bytes 442376 | tf_op jit(solution)/shard_map/ppermute | solution.py:237
  49.8 5.9 %collective-permute-start.20 = (bf16[2,9,32,128]{3,2,1,0:T(8,128)(2,1)S(1)}, bf16[2,9,32,128]{3,2,1,0:T(8,128)(2,1)S(1)}, u32[]{:S(2)}, u32[]{:S(2)}) collective-permute-start(bf16[2,9,32,128]{3,2,1,0:T(8,128)(2,1)S(1)} %get-tuple-element.116), channel_id=1, source_target_pairs={{0,2},{1,5},{2,0},{3,7},{4,6},{5,1},{6,4},{7,3},{8,10},{9,13},{10,... | collective-permute-start | bytes 442376 | tf_op jit(solution)/shard_map/ppermute | solution.py:237
  51.6 20.3 %copy-start.4 = (bf16[8,96,256]{2,1,0:T(8,128)(2,1)S(1)}, bf16[8,96,256]{2,1,0:T(8,128)(2,1)}, u32[]{:S(2)}) copy-start(bf16[8,96,256]{2,1,0:T(8,128)(2,1)} %basis_ref.3) | copy-start | bytes 1179652
  51.6 20.3 %copy-start.5 = (bf16[8,96,96]{2,1,0:T(8,128)(2,1)S(1)}, bf16[8,96,96]{2,1,0:T(8,128)(2,1)}, u32[]{:S(2)}) copy-start(bf16[8,96,96]{2,1,0:T(8,128)(2,1)} %transfer_ref.3) | copy-start | bytes 442372
  51.6 20.3 %copy-start.11 = (s32[12]{0:T(128)S(1)}, s32[12]{0:T(128)}, u32[]{:S(2)}) copy-start(s32[12]{0:T(128)} %ranks_ref.5) | copy-start | bytes 148
  51.6 1.2 collective-permute-start.22
  52.9 1.2 collective-permute-start.23
  54.2 8.5 %collective-permute-start.27 = (bf16[2,9,32,128]{3,2,1,0:T(8,128)(2,1)S(1)}, bf16[2,9,32,128]{3,2,1,0:T(8,128)(2,1)S(1)}, u32[]{:S(2)}, u32[]{:S(2)}) collective-permute-start(bf16[2,9,32,128]{3,2,1,0:T(8,128)(2,1)S(1)} %get-tuple-element.130), channel_id=1, source_target_pairs={{0,14},{1,15},{2,12},{3,13},{4,10},{5,11},{6,8},{7,9},{8,6},{9,7},... | collective-permute-start | bytes 442376 | tf_op jit(solution)/shard_map/ppermute | solution.py:237
  55.9 9.2 %collective-permute-start.24 = (bf16[2,9,32,128]{3,2,1,0:T(8,128)(2,1)S(1)}, bf16[2,9,32,128]{3,2,1,0:T(8,128)(2,1)S(1)}, u32[]{:S(2)}, u32[]{:S(2)}) collective-permute-start(bf16[2,9,32,128]{3,2,1,0:T(8,128)(2,1)S(1)} %get-tuple-element.127), channel_id=1, source_target_pairs={{0,2},{1,5},{2,0},{3,7},{4,6},{5,1},{6,4},{7,3},{8,10},{9,13},{10,... | collective-permute-start | bytes 442376 | tf_op jit(solution)/shard_map/ppermute | solution.py:237
  57.0 8.0 %collective-permute-start.25 = (bf16[2,9,32,128]{3,2,1,0:T(8,128)(2,1)S(1)}, bf16[2,9,32,128]{3,2,1,0:T(8,128)(2,1)S(1)}, u32[]{:S(2)}, u32[]{:S(2)}) collective-permute-start(bf16[2,9,32,128]{3,2,1,0:T(8,128)(2,1)S(1)} %get-tuple-element.128), channel_id=1, source_target_pairs={{0,4},{1,9},{2,6},{3,11},{4,0},{5,13},{6,2},{7,15},{8,12},{9,1},{1... | collective-permute-start | bytes 442376 | tf_op jit(solution)/shard_map/ppermute | solution.py:237
  58.9 6.1 %collective-permute-start.26 = (bf16[2,9,32,128]{3,2,1,0:T(8,128)(2,1)S(1)}, bf16[2,9,32,128]{3,2,1,0:T(8,128)(2,1)S(1)}, u32[]{:S(2)}, u32[]{:S(2)}) collective-permute-start(bf16[2,9,32,128]{3,2,1,0:T(8,128)(2,1)S(1)} %get-tuple-element.129), channel_id=1, source_target_pairs={{0,8},{1,3},{2,10},{3,1},{4,12},{5,7},{6,14},{7,5},{8,0},{9,11},{1... | collective-permute-start | bytes 442376 | tf_op jit(solution)/shard_map/ppermute | solution.py:237
  65.1 6.8 %collective-permute-start.28 = (bf16[9,32,128]{2,1,0:T(8,128)(2,1)S(1)}, bf16[9,32,128]{2,1,0:T(8,128)(2,1)S(1)}, u32[]{:S(2)}, u32[]{:S(2)}) collective-permute-start(bf16[9,32,128]{2,1,0:T(8,128)(2,1)S(1)} %get-tuple-element.132), channel_id=1, source_target_pairs={{0,16},{1,17},{2,18},{3,19},{4,20},{5,21},{6,22},{7,23},{8,24},{9,... | collective-permute-start | bytes 221192 | tf_op jit(solution)/shard_map/ppermute | solution.py:233
  74.5 6.6 %collective-permute-start.29 = (bf16[9,32,128]{2,1,0:T(8,128)(2,1)S(1)}, bf16[9,32,128]{2,1,0:T(8,128)(2,1)S(1)}, u32[]{:S(2)}, u32[]{:S(2)}) collective-permute-start(bf16[9,32,128]{2,1,0:T(8,128)(2,1)S(1)} %get-tuple-element.134.refs_0_), channel_id=1, source_target_pairs={{0,16},{1,17},{2,18},{3,19},{4,20},{5,21},{6,22},{7,23},{8,24},{9,... | collective-permute-start | bytes 221192 | tf_op jit(solution)/shard_map/ppermute | solution.py:233
  81.1 7.6 %collective-permute-start.30 = (bf16[2,9,32,128]{3,2,1,0:T(8,128)(2,1)S(1)}, bf16[2,9,32,128]{3,2,1,0:T(8,128)(2,1)S(1)}, u32[]{:S(2)}, u32[]{:S(2)}) collective-permute-start(bf16[2,9,32,128]{3,2,1,0:T(8,128)(2,1)S(1)} %shard_map.105.refs_0_), channel_id=1, source_target_pairs={{0,2},{1,5},{2,0},{3,7},{4,6},{5,1},{6,4},{7,3},{8,10},{9,13},{10,... | collective-permute-start | bytes 442376 | tf_op jit(solution)/shard_map/ppermute | solution.py:237
  81.2 7.5 %collective-permute-start.31 = (bf16[2,9,32,128]{3,2,1,0:T(8,128)(2,1)S(1)}, bf16[2,9,32,128]{3,2,1,0:T(8,128)(2,1)S(1)}, u32[]{:S(2)}, u32[]{:S(2)}) collective-permute-start(bf16[2,9,32,128]{3,2,1,0:T(8,128)(2,1)S(1)} %shard_map.105.refs_0_), channel_id=1, source_target_pairs={{0,4},{1,9},{2,6},{3,11},{4,0},{5,13},{6,2},{7,15},{8,12},{9,1},{1... | collective-permute-start | bytes 442376 | tf_op jit(solution)/shard_map/ppermute | solution.py:237
  81.9 6.7 %collective-permute-start.32 = (bf16[2,9,32,128]{3,2,1,0:T(8,128)(2,1)S(1)}, bf16[2,9,32,128]{3,2,1,0:T(8,128)(2,1)S(1)}, u32[]{:S(2)}, u32[]{:S(2)}) collective-permute-start(bf16[2,9,32,128]{3,2,1,0:T(8,128)(2,1)S(1)} %shard_map.105.refs_0_), channel_id=1, source_target_pairs={{0,8},{1,3},{2,10},{3,1},{4,12},{5,7},{6,14},{7,5},{8,0},{9,11},{1... | collective-permute-start | bytes 442376 | tf_op jit(solution)/shard_map/ppermute | solution.py:237
  81.9 13.9 %collective-permute-start.36 = (bf16[2,9,32,128]{3,2,1,0:T(8,128)(2,1)S(1)}, bf16[2,9,32,128]{3,2,1,0:T(8,128)(2,1)S(1)}, u32[]{:S(2)}, u32[]{:S(2)}) collective-permute-start(bf16[2,9,32,128]{3,2,1,0:T(8,128)(2,1)S(1)} %shard_map.105.refs_0_), channel_id=1, source_target_pairs={{0,14},{1,15},{2,12},{3,13},{4,10},{5,11},{6,8},{7,9},{8,6},{9,7},... | collective-permute-start | bytes 442376 | tf_op jit(solution)/shard_map/ppermute | solution.py:237
  88.7 7.7 %collective-permute-start.33 = (bf16[2,9,32,128]{3,2,1,0:T(8,128)(2,1)S(1)}, bf16[2,9,32,128]{3,2,1,0:T(8,128)(2,1)S(1)}, u32[]{:S(2)}, u32[]{:S(2)}) collective-permute-start(bf16[2,9,32,128]{3,2,1,0:T(8,128)(2,1)S(1)} %collective-permute-done.30.refs_1_), channel_id=1, source_target_pairs={{0,4},{1,9},{2,6},{3,11},{4,0},{5,13},{6,2},{7,15},{8,12},{9,1},{1... | collective-permute-start | bytes 442376 | tf_op jit(solution)/shard_map/ppermute | solution.py:237
  90.0 5.8 %collective-permute-start.37 = (bf16[1,32,256]{2,1,0:T(8,128)(2,1)S(1)}, bf16[1,32,256]{2,1,0:T(8,128)(2,1)S(1)}, u32[]{:S(2)}, u32[]{:S(2)}) collective-permute-start(bf16[1,32,256]{2,1,0:T(8,128)(2,1)S(1)} %get-tuple-element.139), channel_id=1, source_target_pairs={{1,3},{3,5},{5,7},{7,9},{9,11},{11,13},{13,15},{15,17},{17,19},{19... | collective-permute-start | bytes 49160 | tf_op jit(solution)/shard_map/ppermute | solution.py:355
  91.3 6.6 %collective-permute-start.34 = (bf16[2,9,32,128]{3,2,1,0:T(8,128)(2,1)S(1)}, bf16[2,9,32,128]{3,2,1,0:T(8,128)(2,1)S(1)}, u32[]{:S(2)}, u32[]{:S(2)}) collective-permute-start(bf16[2,9,32,128]{3,2,1,0:T(8,128)(2,1)S(1)} %collective-permute-done.32.refs_4_), channel_id=1, source_target_pairs={{0,2},{1,5},{2,0},{3,7},{4,6},{5,1},{6,4},{7,3},{8,10},{9,13},{10,... | collective-permute-start | bytes 442376 | tf_op jit(solution)/shard_map/ppermute | solution.py:237
  94.0 5.1 %collective-permute-start.35 = (bf16[2,9,32,128]{3,2,1,0:T(8,128)(2,1)S(1)}, bf16[2,9,32,128]{3,2,1,0:T(8,128)(2,1)S(1)}, u32[]{:S(2)}, u32[]{:S(2)}) collective-permute-start(bf16[2,9,32,128]{3,2,1,0:T(8,128)(2,1)S(1)} %collective-permute-done.31.refs_2_), channel_id=1, source_target_pairs={{0,8},{1,3},{2,10},{3,1},{4,12},{5,7},{6,14},{7,5},{8,0},{9,11},{1... | collective-permute-start | bytes 442376 | tf_op jit(solution)/shard_map/ppermute | solution.py:237
  95.8 3.3 %collective-permute-start.38 = (bf16[2,9,32,128]{3,2,1,0:T(8,128)(2,1)S(1)}, bf16[2,9,32,128]{3,2,1,0:T(8,128)(2,1)S(1)}, u32[]{:S(2)}, u32[]{:S(2)}) collective-permute-start(bf16[2,9,32,128]{3,2,1,0:T(8,128)(2,1)S(1)} %shard_map.105.refs_0_), channel_id=1, source_target_pairs={{0,1},{1,0},{2,3},{3,2},{4,5},{5,4},{6,7},{7,6},{8,9},{9,8},{10,11... | collective-permute-start | bytes 442376 | tf_op jit(solution)/shard_map/ppermute | solution.py:242
  95.8 3.8 %collective-permute-start.39 = (bf16[2,9,32,128]{3,2,1,0:T(8,128)(2,1)S(1)}, bf16[2,9,32,128]{3,2,1,0:T(8,128)(2,1)S(1)}, u32[]{:S(2)}, u32[]{:S(2)}) collective-permute-start(bf16[2,9,32,128]{3,2,1,0:T(8,128)(2,1)S(1)} %collective-permute-done.30.refs_1_), channel_id=1, source_target_pairs={{0,1},{1,0},{2,3},{3,2},{4,5},{5,4},{6,7},{7,6},{8,9},{9,8},{10,11... | collective-permute-start | bytes 442376 | tf_op jit(solution)/shard_map/ppermute | solution.py:242
  96.3 3.4 %collective-permute-start.40 = (bf16[2,9,32,128]{3,2,1,0:T(8,128)(2,1)S(1)}, bf16[2,9,32,128]{3,2,1,0:T(8,128)(2,1)S(1)}, u32[]{:S(2)}, u32[]{:S(2)}) collective-permute-start(bf16[2,9,32,128]{3,2,1,0:T(8,128)(2,1)S(1)} %collective-permute-done.31.refs_2_), channel_id=1, source_target_pairs={{0,1},{1,0},{2,3},{3,2},{4,5},{5,4},{6,7},{7,6},{8,9},{9,8},{10,11... | collective-permute-start | bytes 442376 | tf_op jit(solution)/shard_map/ppermute | solution.py:242
  97.9 2.3 %collective-permute-start.42 = (bf16[2,9,32,128]{3,2,1,0:T(8,128)(2,1)S(1)}, bf16[2,9,32,128]{3,2,1,0:T(8,128)(2,1)S(1)}, u32[]{:S(2)}, u32[]{:S(2)}) collective-permute-start(bf16[2,9,32,128]{3,2,1,0:T(8,128)(2,1)S(1)} %collective-permute-done.32.refs_4_), channel_id=1, source_target_pairs={{0,1},{1,0},{2,3},{3,2},{4,5},{5,4},{6,7},{7,6},{8,9},{9,8},{10,11... | collective-permute-start | bytes 442376 | tf_op jit(solution)/shard_map/ppermute | solution.py:242
  99.1 1.4 %collective-permute-start.41 = (bf16[2,9,32,128]{3,2,1,0:T(8,128)(2,1)S(1)}, bf16[2,9,32,128]{3,2,1,0:T(8,128)(2,1)S(1)}, u32[]{:S(2)}, u32[]{:S(2)}) collective-permute-start(bf16[2,9,32,128]{3,2,1,0:T(8,128)(2,1)S(1)} %collective-permute-done.33.refs_3_), channel_id=1, source_target_pairs={{0,1},{1,0},{2,3},{3,2},{4,5},{5,4},{6,7},{7,6},{8,9},{9,8},{10,11... | collective-permute-start | bytes 442376 | tf_op jit(solution)/shard_map/ppermute | solution.py:242
  99.2 1.6 %collective-permute-start.43 = (bf16[2,9,32,128]{3,2,1,0:T(8,128)(2,1)S(1)}, bf16[2,9,32,128]{3,2,1,0:T(8,128)(2,1)S(1)}, u32[]{:S(2)}, u32[]{:S(2)}) collective-permute-start(bf16[2,9,32,128]{3,2,1,0:T(8,128)(2,1)S(1)} %collective-permute-done.34.refs_5_), channel_id=1, source_target_pairs={{0,1},{1,0},{2,3},{3,2},{4,5},{5,4},{6,7},{7,6},{8,9},{9,8},{10,11... | collective-permute-start | bytes 442376 | tf_op jit(solution)/shard_map/ppermute | solution.py:242
  99.7 1.4 %collective-permute-start.44 = (bf16[2,9,32,128]{3,2,1,0:T(8,128)(2,1)S(1)}, bf16[2,9,32,128]{3,2,1,0:T(8,128)(2,1)S(1)}, u32[]{:S(2)}, u32[]{:S(2)}) collective-permute-start(bf16[2,9,32,128]{3,2,1,0:T(8,128)(2,1)S(1)} %collective-permute-done.35.refs_6_), channel_id=1, source_target_pairs={{0,1},{1,0},{2,3},{3,2},{4,5},{5,4},{6,7},{7,6},{8,9},{9,8},{10,11... | collective-permute-start | bytes 442376 | tf_op jit(solution)/shard_map/ppermute | solution.py:242
  99.7 1.5 %collective-permute-start.45 = (bf16[2,9,32,128]{3,2,1,0:T(8,128)(2,1)S(1)}, bf16[2,9,32,128]{3,2,1,0:T(8,128)(2,1)S(1)}, u32[]{:S(2)}, u32[]{:S(2)}) collective-permute-start(bf16[2,9,32,128]{3,2,1,0:T(8,128)(2,1)S(1)} %collective-permute-done.36.refs_7_), channel_id=1, source_target_pairs={{0,1},{1,0},{2,3},{3,2},{4,5},{5,4},{6,7},{7,6},{8,9},{9,8},{10,11... | collective-permute-start | bytes 442376 | tf_op jit(solution)/shard_map/ppermute | solution.py:242
  106.6 2.1 %collective-permute-start.46 = (bf16[4,2,9,32,128]{4,3,2,1,0:T(8,128)(2,1)S(1)}, bf16[4,2,9,32,128]{4,3,2,1,0:T(8,128)(2,1)S(1)}, u32[]{:S(2)}, u32[]{:S(2)}) collective-permute-start(bf16[4,2,9,32,128]{4,3,2,1,0:T(8,128)(2,1)S(1)} %get-tuple-element.151), channel_id=1, source_target_pairs={{0,1},{1,0},{2,3},{3,2},{4,5},{5,4},{6,7},{7,6},{8,9},{9,8},{10,11... | collective-permute-start | bytes 1769480 | tf_op jit(solution)/shard_map/ppermute | solution.py:242
  108.8 7.9 %collective-permute-start.50 = (bf16[4,2,9,32,128]{4,3,2,1,0:T(8,128)(2,1)S(1)}, bf16[4,2,9,32,128]{4,3,2,1,0:T(8,128)(2,1)S(1)}, u32[]{:S(2)}, u32[]{:S(2)}) collective-permute-start(bf16[4,2,9,32,128]{4,3,2,1,0:T(8,128)(2,1)S(1)} %get-tuple-element.160), channel_id=1, source_target_pairs={{0,1},{1,0},{2,3},{3,2},{4,5},{5,4},{6,7},{7,6},{8,9},{9,8},{10,11... | collective-permute-start | bytes 1769480 | tf_op jit(solution)/shard_map/ppermute | solution.py:242
  109.2 7.5 %collective-permute-start.47 = (bf16[2,9,32,128]{3,2,1,0:T(8,128)(2,1)S(1)}, bf16[2,9,32,128]{3,2,1,0:T(8,128)(2,1)S(1)}, u32[]{:S(2)}, u32[]{:S(2)}) collective-permute-start(bf16[2,9,32,128]{3,2,1,0:T(8,128)(2,1)S(1)} %get-tuple-element.157), channel_id=1, source_target_pairs={{0,4},{1,9},{2,6},{3,11},{4,0},{5,13},{6,2},{7,15},{8,12},{9,1},{1... | collective-permute-start | bytes 442376 | tf_op jit(solution)/shard_map/ppermute | solution.py:237
  109.9 6.8 %collective-permute-start.48 = (bf16[2,9,32,128]{3,2,1,0:T(8,128)(2,1)S(1)}, bf16[2,9,32,128]{3,2,1,0:T(8,128)(2,1)S(1)}, u32[]{:S(2)}, u32[]{:S(2)}) collective-permute-start(bf16[2,9,32,128]{3,2,1,0:T(8,128)(2,1)S(1)} %get-tuple-element.158), channel_id=1, source_target_pairs={{0,8},{1,3},{2,10},{3,1},{4,12},{5,7},{6,14},{7,5},{8,0},{9,11},{1... | collective-permute-start | bytes 442376 | tf_op jit(solution)/shard_map/ppermute | solution.py:237
  110.7 6.0 %collective-permute-start.49 = (bf16[2,9,32,128]{3,2,1,0:T(8,128)(2,1)S(1)}, bf16[2,9,32,128]{3,2,1,0:T(8,128)(2,1)S(1)}, u32[]{:S(2)}, u32[]{:S(2)}) collective-permute-start(bf16[2,9,32,128]{3,2,1,0:T(8,128)(2,1)S(1)} %get-tuple-element.159), channel_id=1, source_target_pairs={{0,2},{1,5},{2,0},{3,7},{4,6},{5,1},{6,4},{7,3},{8,10},{9,13},{10,... | collective-permute-start | bytes 442376 | tf_op jit(solution)/shard_map/ppermute | solution.py:237
  112.3 1.2 collective-permute-start.51
  113.5 1.2 collective-permute-start.52
  114.8 8.5 %collective-permute-start.56 = (bf16[2,9,32,128]{3,2,1,0:T(8,128)(2,1)S(1)}, bf16[2,9,32,128]{3,2,1,0:T(8,128)(2,1)S(1)}, u32[]{:S(2)}, u32[]{:S(2)}) collective-permute-start(bf16[2,9,32,128]{3,2,1,0:T(8,128)(2,1)S(1)} %get-tuple-element.173), channel_id=1, source_target_pairs={{0,14},{1,15},{2,12},{3,13},{4,10},{5,11},{6,8},{7,9},{8,6},{9,7},... | collective-permute-start | bytes 442376 | tf_op jit(solution)/shard_map/ppermute | solution.py:237
  116.9 8.8 %collective-permute-start.53 = (bf16[2,9,32,128]{3,2,1,0:T(8,128)(2,1)S(1)}, bf16[2,9,32,128]{3,2,1,0:T(8,128)(2,1)S(1)}, u32[]{:S(2)}, u32[]{:S(2)}) collective-permute-start(bf16[2,9,32,128]{3,2,1,0:T(8,128)(2,1)S(1)} %get-tuple-element.170), channel_id=1, source_target_pairs={{0,2},{1,5},{2,0},{3,7},{4,6},{5,1},{6,4},{7,3},{8,10},{9,13},{10,... | collective-permute-start | bytes 442376 | tf_op jit(solution)/shard_map/ppermute | solution.py:237
  117.7 8.0 %collective-permute-start.54 = (bf16[2,9,32,128]{3,2,1,0:T(8,128)(2,1)S(1)}, bf16[2,9,32,128]{3,2,1,0:T(8,128)(2,1)S(1)}, u32[]{:S(2)}, u32[]{:S(2)}) collective-permute-start(bf16[2,9,32,128]{3,2,1,0:T(8,128)(2,1)S(1)} %get-tuple-element.171), channel_id=1, source_target_pairs={{0,4},{1,9},{2,6},{3,11},{4,0},{5,13},{6,2},{7,15},{8,12},{9,1},{1... | collective-permute-start | bytes 442376 | tf_op jit(solution)/shard_map/ppermute | solution.py:237
  119.5 6.2 %collective-permute-start.55 = (bf16[2,9,32,128]{3,2,1,0:T(8,128)(2,1)S(1)}, bf16[2,9,32,128]{3,2,1,0:T(8,128)(2,1)S(1)}, u32[]{:S(2)}, u32[]{:S(2)}) collective-permute-start(bf16[2,9,32,128]{3,2,1,0:T(8,128)(2,1)S(1)} %get-tuple-element.172), channel_id=1, source_target_pairs={{0,8},{1,3},{2,10},{3,1},{4,12},{5,7},{6,14},{7,5},{8,0},{9,11},{1... | collective-permute-start | bytes 442376 | tf_op jit(solution)/shard_map/ppermute | solution.py:237
  125.8 6.4 %collective-permute-start.57 = (bf16[9,32,128]{2,1,0:T(8,128)(2,1)S(1)}, bf16[9,32,128]{2,1,0:T(8,128)(2,1)S(1)}, u32[]{:S(2)}, u32[]{:S(2)}) collective-permute-start(bf16[9,32,128]{2,1,0:T(8,128)(2,1)S(1)} %get-tuple-element.175), channel_id=1, source_target_pairs={{0,16},{1,17},{2,18},{3,19},{4,20},{5,21},{6,22},{7,23},{8,24},{9,... | collective-permute-start | bytes 221192 | tf_op jit(solution)/shard_map/ppermute | solution.py:233
  (10 other events, 41.5 us)

commit v12 on v11

--- a/solution.py
+++ b/solution.py
@@ -162,6 +162,10 @@
     for n, (part_ref, out_ref) in enumerate(zip(part_refs, out_refs)):
         total = keep_ref[n + 1].astype(F32) + swap_ref[n + 1].astype(F32)
         out_ref[...] = (total + part_ref[...].astype(F32)).astype(BF)
+
+
+def pick_kernel(flag_ref, first_ref, second_ref, out_ref):
+    out_ref[...] = jnp.where(flag_ref[0] == 0, first_ref[...], second_ref[...])
 
 
 def join_kernel(*refs):
@@ -276,7 +280,7 @@
 
     order = ((x | y | z, x | y, y | z, z | x), (0, x, y, z))
     couple = pl.pallas_call(
-        functools.partial(couple_kernel, order=order, unroll=8),
+        functools.partial(couple_kernel, order=order, unroll=32),
         out_shape=[shape((4, far) + tile_shape, BF)] * 4,
         in_specs=[SMEM, SMEM, VMEM] + [VMEM] * (cores * chips),
         out_specs=[VMEM] * 4,
@@ -342,19 +346,36 @@
             compiler_params=params(16),
         )
 
-    halo_pairs = [(d, d + cores) for d in range(1, devices - cores, cores)]
-    halo_pairs += [(d, d - cores) for d in range(cores, devices, cores)]
+    count = devices // cores
+    halo_pairs = []
+    for parity in range(2):
+        chain = [(c, c + 1) for c in range(parity, count - 1, 2)]
+        halo_pairs.append([(a * cores + k, b * cores + k) for p in chain for a, b in (p, p[::-1]) for k in range(cores)])
+    halo_turn = ((me // cores + core) % 2).reshape(1)
+    pick = pl.pallas_call(
+        pick_kernel, out_shape=edge_shape, in_specs=[SMEM, VMEM, VMEM], out_specs=VMEM, compiler_params=params(1)
+    )
+
+    def swap_halo(edge_row):
+        return [lax.ppermute(edge_row, "clu", pairs) for pairs in halo_pairs]
 
     def apply_matrix(field_in, coeffs, inner, outer, coupling, with_coeffs):
-        (column,) = join(coeffs, *[swap_far(coeffs, s) for s in range(1, far)])
+        away = [swap_far(coeffs, s) for s in range(1, far)]
+        if with_coeffs:
+            away, coupling = barrier((away, coupling))
+        else:
+            away, outer = barrier((away, swap_halo(outer)))
+        (column,) = join(coeffs, *away)
         got = {0: column, x: swap(column, x), y: swap(column, y), z: swap(column, z)}
-        got, coupling = barrier((got, coupling))
+        if with_coeffs:
+            got, outer = barrier((got, swap_halo(outer)))
+        else:
+            got = barrier(got)
         corner = swap(column, x | y | z)
         other = {chip: swap_cores(part) for chip, part in got.items()}
         got |= {x | y: swap(got[x], y), y | z: swap(got[y], z), z | x: swap(got[z], x)}
-        outer = lax.ppermute(outer, "clu", halo_pairs)
         near_sum = near(field_in, near_field)
-        got, corner, outer, near_sum = barrier((got, corner, outer, near_sum))
+        got, corner, near_sum = barrier((got, corner, near_sum))
         got[x | y | z] = corner
         other |= {chip: swap_cores(got[chip]) for chip in order[0]}
         keep_long, keep, send_long, send = couple(
@@ -366,11 +387,15 @@
         )
         corner, xy, yz, zx = far_add(keep_long, swap_cores(send_long))
         corner, xy, yz, zx, send = barrier((corner, xy, yz, zx, send))
-        inner, outer = swap_cores(inner), swap_cores(outer)
-        edges = edge(core_index, inner, outer, near_field, near_field)
-        to_x, to_y, to_z, swapped, edges = barrier((swap(xy, y), swap(yz, z), swap(zx, x), swap_cores(send), edges))
-        own, to_x, to_y, to_z = middle_add(keep, swapped, to_x, to_y, to_z)
-        total, *away = last_add(own, swap(to_x, x), swap(to_y, y), swap(to_z, z), swap(corner, x | y | z))
+        to_x, to_y, to_z, swapped = barrier((swap(xy, y), swap(yz, z), swap(zx, x), swap_cores(send)))
+        own, to_x, to_y, to_z, inner, outer = barrier(
+            (*middle_add(keep, swapped, to_x, to_y, to_z), inner, pick(halo_turn, *outer))
+        )
+        edges = edge(core_index, swap_cores(inner), swap_cores(outer), near_field, near_field)
+        own, to_x, to_y, to_z, corner, edges = barrier(
+            (own, swap(to_x, x), swap(to_y, y), swap(to_z, z), swap(corner, x | y | z), edges)
+        )
+        total, *away = last_add(own, to_x, to_y, to_z, corner)
         terms = [swap_far(part, s + 1) for s, part in enumerate(away)]
         return finish(with_coeffs)(ranks, core_index, near_sum, edges, basis, transfer, total, *terms)
 

time: 135 us -> 140 us (1.037)
  starting transfers between devices: 52.8 us -> 60.5 us
  waiting for transfers between devices: 48.5 us -> 41 us
  local copies, waits for them, and re-layouts: 10.8 us -> 14.7 us
    ppermute x4, waiting for transfers between devices: 20.1 us -> 10.7 us  [swap_far(): lax.ppermute(part, 'clu', [(d, (d + shift * cube) % devices) for d in ran...]
    ppermute x28, starting transfers between devices: 36.7 us -> 42.3 us  [swap(): lax.ppermute(part, 'clu', [(d, d ^ (turned if d % cores else direction) *...]
    ppermute x2 -> x4, starting transfers between devices: 2.56 us -> 7.85 us  [swap_halo(): return [lax.ppermute(edge_row, 'clu', pairs) for pairs in halo_pairs]]
    unnamed x32 -> x50, local copies, waits for them, and re-layouts: 6.02 us -> 9.95 us
    ppermute x4, starting transfers between devices: 7.89 us -> 5.07 us  [swap_far(): lax.ppermute(part, 'clu', [(d, (d + shift * cube) % devices) for d in ran...]
    ppermute x28, waiting for transfers between devices: 16.4 us -> 19.2 us  [swap(): lax.ppermute(part, 'clu', [(d, d ^ (turned if d % cores else direction) *...]
    pallas_call x2, Pallas kernels: 11.5 us -> 9.39 us  [apply_matrix(): couple(source_rows, target_rows, coupling, *[got[chip] for chip in range(...]
  transfers between devices with their start and end apart: 58 -> 60, of which waited for: 27 -> 31; matrix products, arithmetic and copies ran while one was open for 4% -> 4% of each run, Pallas kernels for 1% -> 2%
where the time goes in v12:
time: 140 us; the launch traced here: 139 us
  starting transfers between devices  60.5 us (43%)
  waiting for transfers between devices  41 us (29%)
  Pallas kernels  21.4 us (15%)
  local copies, waits for them, and re-layouts  14.7 us (10%)
    ppermute x28, starting transfers between devices, swap(): lax.ppermute(part, 'clu', [(d, d ^ (turned if d % cores else direction) *...  42.3 us
    ppermute x28, waiting for transfers between devices, swap(): lax.ppermute(part, 'clu', [(d, d ^ (turned if d % cores else direction) *...  19.2 us
    ppermute x4, waiting for transfers between devices, swap_far(): lax.ppermute(part, 'clu', [(d, (d + shift * cube) % devices) for d in ran...  10.7 us
    unnamed x50, local copies, waits for them, and re-layouts  9.95 us
    ppermute x24, waiting for transfers between devices, swap_cores(): return lax.ppermute(part, 'clu', [(d, d ^ 1) for d in range(devices)])  9.4 us
    pallas_call x2, Pallas kernels, apply_matrix(): couple(source_rows, target_rows, coupling, *[got[chip] for chip in range(...  9.39 us
    ppermute x4, starting transfers between devices, swap_halo(): return [lax.ppermute(edge_row, 'clu', pairs) for pairs in halo_pairs]  7.85 us
    ppermute x24, starting transfers between devices, swap_cores(): return lax.ppermute(part, 'clu', [(d, d ^ 1) for d in range(devices)])  5.21 us
  transfers between devices with their start and end apart: 60, of which 31 were waited for; matrix products, arithmetic and copies ran while one was open for 4% of the time, Pallas kernels for 2%

profile of v12, /device:TPU:0, one launch (start us, length us, event | category | flops | bytes accessed | tf_op | source)
XLA Modules:
  0.0 139.3 jit_solution(12056734566742414174)
XLA Ops:
  0.6 2.9 %shard_map.95 = (bf16[9,32,128]{2,1,0:T(8,128)(2,1)}, bf16[1,32,256]{2,1,0:T(8,128)(2,1)}, bf16[1,32,256]{2,1,0:T(8,128)(2,1)}) custom-call(s32[12]{0:T(128)} %ranks_ref.5, s32[1]{0:T(128)} %bitcast.core_ref, bf16[8,32,256]{2,1,0:T(8,128)(2,1)} %v_ref.1, bf16[8,96,256]{2,1,0:T(8,128)(2,1)} %basis_ref.3, bf16[8,96,96]{2,1,0:T(8,128)(2,1)} %transfer_ref.3), custom_call_target="tpu_custom_call" | custom-call | tf_op jit(solution)/shard_map/pallas_call | solution.py:268
  3.5 4.1 %collective-permute-start = (bf16[9,32,128]{2,1,0:T(8,128)(2,1)}, bf16[9,32,128]{2,1,0:T(8,128)(2,1)S(1)}, u32[]{:S(2)}, u32[]{:S(2)}) collective-permute-start(bf16[9,32,128]{2,1,0:T(8,128)(2,1)} %get-tuple-element.115.refs_0_), channel_id=1, source_target_pairs={{0,16},{1,17},{2,18},{3,19},{4,20},{5,21},{6,22},{7,23},{8,24},{9,... | collective-permute-start | bytes 221192 | tf_op jit(solution)/shard_map/ppermute | solution.py:237
  7.6 4.8 %copy.11.in_ref = bf16[128,96,96]{2,1,0:T(8,128)(2,1)} copy(bf16[128,96,96]{0,2,1:T(8,128)(2,1)} %param.12) | data formatting | bytes 4718592 | tf_op jit(solution)/shard_map/optimization_barrier | solution.py:402
  12.4 1.9 %copy-done.1 = bf16[128,96,96]{2,1,0:T(8,128)(2,1)S(1)} copy-done((bf16[128,96,96]{2,1,0:T(8,128)(2,1)S(1)}, bf16[128,96,96]{2,1,0:T(8,128)(2,1)}, u32[]{:S(2)}) %copy-start.1) | copy-done | bytes 2359320
  14.3 1.6 %copy-done.2 = bf16[128,96,96]{2,1,0:T(8,128)(2,1)} copy-done((bf16[128,96,96]{2,1,0:T(8,128)(2,1)}, bf16[128,96,96]{2,1,0:T(8,128)(2,1)S(1)}, u32[]{:S(2)}) %copy-start.2) | copy-done | bytes 2359320
  16.0 1.6 %collective-permute-start.3 = (bf16[2,9,32,128]{3,2,1,0:T(8,128)(2,1)S(1)}, bf16[2,9,32,128]{3,2,1,0:T(8,128)(2,1)}, u32[]{:S(2)}, u32[]{:S(2)}) collective-permute-start(bf16[2,9,32,128]{3,2,1,0:T(8,128)(2,1)S(1)} %shard_map.97.refs_0_), channel_id=1, source_target_pairs={{0,8},{1,3},{2,10},{3,1},{4,12},{5,7},{6,14},{7,5},{8,0},{9,11},{1... | collective-permute-start | bytes 442376 | tf_op jit(solution)/shard_map/ppermute | solution.py:241
  17.6 1.5 %collective-permute-start.2 = (bf16[2,9,32,128]{3,2,1,0:T(8,128)(2,1)S(1)}, bf16[2,9,32,128]{3,2,1,0:T(8,128)(2,1)}, u32[]{:S(2)}, u32[]{:S(2)}) collective-permute-start(bf16[2,9,32,128]{3,2,1,0:T(8,128)(2,1)S(1)} %shard_map.97.refs_0_), channel_id=1, source_target_pairs={{0,4},{1,9},{2,6},{3,11},{4,0},{5,13},{6,2},{7,15},{8,12},{9,1},{1... | collective-permute-start | bytes 442376 | tf_op jit(solution)/shard_map/ppermute | solution.py:241
  19.1 1.5 %collective-permute-start.1 = (bf16[2,9,32,128]{3,2,1,0:T(8,128)(2,1)S(1)}, bf16[2,9,32,128]{3,2,1,0:T(8,128)(2,1)}, u32[]{:S(2)}, u32[]{:S(2)}) collective-permute-start(bf16[2,9,32,128]{3,2,1,0:T(8,128)(2,1)S(1)} %shard_map.97.refs_0_), channel_id=1, source_target_pairs={{0,2},{1,5},{2,0},{3,7},{4,6},{5,1},{6,4},{7,3},{8,10},{9,13},{10,... | collective-permute-start | bytes 442376 | tf_op jit(solution)/shard_map/ppermute | solution.py:241
  21.3 3.3 %collective-permute-start.4 = (bf16[1,32,256]{2,1,0:T(8,128)(2,1)S(1)}, bf16[1,32,256]{2,1,0:T(8,128)(2,1)S(1)}, u32[]{:S(2)}, u32[]{:S(2)}) collective-permute-start(bf16[1,32,256]{2,1,0:T(8,128)(2,1)S(1)} %copy-done.24), channel_id=1, source_target_pairs={{0,2},{1,3},{2,0},{3,1},{4,6},{5,7},{6,4},{7,5},{8,10},{9,11},{10,... | collective-permute-start | bytes 49160 | tf_op jit(solution)/shard_map/ppermute | solution.py:360
  25.1 3.8 %collective-permute-start.9 = (bf16[2,9,32,128]{3,2,1,0:T(8,128)(2,1)S(1)}, bf16[2,9,32,128]{3,2,1,0:T(8,128)(2,1)S(1)}, u32[]{:S(2)}, u32[]{:S(2)}) collective-permute-start(bf16[2,9,32,128]{3,2,1,0:T(8,128)(2,1)S(1)} %shard_map.97.refs_0_), channel_id=1, source_target_pairs={{0,14},{1,15},{2,12},{3,13},{4,10},{5,11},{6,8},{7,9},{8,6},{9,7},... | collective-permute-start | bytes 442376 | tf_op jit(solution)/shard_map/ppermute | solution.py:241
  29.0 0.7 collective-permute-start.6
  29.7 1.6 %collective-permute-start.8 = (bf16[2,9,32,128]{3,2,1,0:T(8,128)(2,1)}, bf16[2,9,32,128]{3,2,1,0:T(8,128)(2,1)}, u32[]{:S(2)}, u32[]{:S(2)}) collective-permute-start(bf16[2,9,32,128]{3,2,1,0:T(8,128)(2,1)} %collective-permute-done.2.refs_2_), channel_id=1, source_target_pairs={{0,8},{1,3},{2,10},{3,1},{4,12},{5,7},{6,14},{7,5},{8,0},{9,11},{1... | collective-permute-start | bytes 442376 | tf_op jit(solution)/shard_map/ppermute | solution.py:241
  31.3 0.8 collective-permute-start.7
  32.1 1.1 collective-permute-done.9.refs_7_
  33.2 2.2 %collective-permute-done.6.refs_3_ = bf16[2,9,32,128]{3,2,1,0:T(8,128)(2,1)} collective-permute-done((bf16[2,9,32,128]{3,2,1,0:T(8,128)(2,1)}, bf16[2,9,32,128]{3,2,1,0:T(8,128)(2,1)}, u32[]{:S(2)}, u32[]{:S(2)}) %collective-permute-start.6) | collective-permute-done | bytes 147488 | tf_op jit(solution)/shard_map/ppermute | solution.py:241
  35.4 0.9 copy-done.9
  38.5 0.7 fusion.1
  39.6 5.5 %shard_map.99 = (bf16[4,2,9,32,128]{4,3,2,1,0:T(8,128)(2,1)S(1)}, bf16[4,2,9,32,128]{4,3,2,1,0:T(8,128)(2,1)S(1)}, bf16[4,2,9,32,128]{4,3,2,1,0:T(8,128)(2,1)S(1)}, bf16[4,2,9,32,128]{4,3,2,1,0:T(8,128)(2,1)}) custom-call(s32[128]{0:T(128)S(1)} %get-tuple-element.226.source_ref, s32[128]{0:T(128)S(1)} %get-tuple-element.227.target_ref, ...), custom_call_target="tpu_custom_call" | custom-call | flops 75497472 | bytes 10485760 | tf_op jit(solution)/shard_map/pallas_call | solution.py:381
  45.1 0.8 copy-done.7
  46.3 1.7 %collective-permute-done.18.swap_ref = bf16[4,2,9,32,128]{4,3,2,1,0:T(8,128)(2,1)S(1)} collective-permute-done((bf16[4,2,9,32,128]{4,3,2,1,0:T(8,128)(2,1)S(1)}, bf16[4,2,9,32,128]{4,3,2,1,0:T(8,128)(2,1)S(1)}, u32[]{:S(2)}, u32[]{:S(2)}) %collective-permute-start.18) | collective-permute-done | bytes 589856 | tf_op jit(solution)/shard_map/ppermute | solution.py:246
  47.9 0.8 shard_map.100
  49.7 1.4 %collective-permute-start.19 = (bf16[2,9,32,128]{3,2,1,0:T(8,128)(2,1)}, bf16[2,9,32,128]{3,2,1,0:T(8,128)(2,1)S(1)}, u32[]{:S(2)}, u32[]{:S(2)}) collective-permute-start(bf16[2,9,32,128]{3,2,1,0:T(8,128)(2,1)} %get-tuple-element.141), channel_id=1, source_target_pairs={{0,4},{1,9},{2,6},{3,11},{4,0},{5,13},{6,2},{7,15},{8,12},{9,1},{1... | collective-permute-start | bytes 442376 | tf_op jit(solution)/shard_map/ppermute | solution.py:241
  51.2 1.7 %collective-permute-start.20 = (bf16[2,9,32,128]{3,2,1,0:T(8,128)(2,1)}, bf16[2,9,32,128]{3,2,1,0:T(8,128)(2,1)}, u32[]{:S(2)}, u32[]{:S(2)}) collective-permute-start(bf16[2,9,32,128]{3,2,1,0:T(8,128)(2,1)} %get-tuple-element.142), channel_id=1, source_target_pairs={{0,8},{1,3},{2,10},{3,1},{4,12},{5,7},{6,14},{7,5},{8,0},{9,11},{1... | collective-permute-start | bytes 442376 | tf_op jit(solution)/shard_map/ppermute | solution.py:241
  53.1 0.7 copy-done.15
  53.8 0.7 copy-done.17
  54.5 1.8 %collective-permute-start.26 = (bf16[2,9,32,128]{3,2,1,0:T(8,128)(2,1)}, bf16[2,9,32,128]{3,2,1,0:T(8,128)(2,1)S(1)}, u32[]{:S(2)}, u32[]{:S(2)}) collective-permute-start(bf16[2,9,32,128]{3,2,1,0:T(8,128)(2,1)} %copy-done.23), channel_id=1, source_target_pairs={{0,14},{1,15},{2,12},{3,13},{4,10},{5,11},{6,8},{7,9},{8,6},{9,7},... | collective-permute-start | bytes 442376 | tf_op jit(solution)/shard_map/ppermute | solution.py:241
  56.6 1.7 %collective-permute-done.21.refs_2_ = bf16[2,9,32,128]{3,2,1,0:T(8,128)(2,1)} collective-permute-done((bf16[2,9,32,128]{3,2,1,0:T(8,128)(2,1)}, bf16[2,9,32,128]{3,2,1,0:T(8,128)(2,1)}, u32[]{:S(2)}, u32[]{:S(2)}) %collective-permute-start.21) | collective-permute-done | bytes 147488 | tf_op jit(solution)/shard_map/ppermute | solution.py:241
  58.3 1.1 copy-done.8
  59.4 1.4 shard_map.101
  61.1 4.2 %collective-permute-start.24 = (bf16[2,9,32,128]{3,2,1,0:T(8,128)(2,1)S(1)}, bf16[2,9,32,128]{3,2,1,0:T(8,128)(2,1)S(1)}, u32[]{:S(2)}, u32[]{:S(2)}) collective-permute-start(bf16[2,9,32,128]{3,2,1,0:T(8,128)(2,1)S(1)} %get-tuple-element.158), channel_id=1, source_target_pairs={{0,4},{1,9},{2,6},{3,11},{4,0},{5,13},{6,2},{7,15},{8,12},{9,1},{1... | collective-permute-start | bytes 442376 | tf_op jit(solution)/shard_map/ppermute | solution.py:241
  65.3 1.4 collective-permute-done.27.inner_ref
  66.8 1.0 collective-permute-done.28.outer_ref
  68.4 2.0 %collective-permute-done.25.refs_2_ = bf16[2,9,32,128]{3,2,1,0:T(8,128)(2,1)S(1)} collective-permute-done((bf16[2,9,32,128]{3,2,1,0:T(8,128)(2,1)S(1)}, bf16[2,9,32,128]{3,2,1,0:T(8,128)(2,1)S(1)}, u32[]{:S(2)}, u32[]{:S(2)}) %collective-permute-start.25) | collective-permute-done | bytes 147488 | tf_op jit(solution)/shard_map/ppermute | solution.py:241
  70.6 5.5 %collective-permute-done.29.rest_0_ = bf16[9,32,128]{2,1,0:T(8,128)(2,1)S(1)} collective-permute-done((bf16[9,32,128]{2,1,0:T(8,128)(2,1)S(1)}, bf16[9,32,128]{2,1,0:T(8,128)(2,1)S(1)}, u32[]{:S(2)}, u32[]{:S(2)}) %collective-permute-start.29) | collective-permute-done | bytes 73760 | tf_op jit(solution)/shard_map/ppermute | solution.py:237
  76.1 2.5 %shard_map.105 = (bf16[8,32,256]{2,1,0:T(8,128)(2,1)}, bf16[9,32,128]{2,1,0:T(8,128)(2,1)S(1)}, bf16[1,32,256]{2,1,0:T(8,128)(2,1)S(1)}, bf16[1,32,256]{2,1,0:T(8,128)(2,1)S(1)}) custom-call(s32[12]{0:T(128)S(1)} %copy-done.22, s32[1]{0:T(128)} %bitcast.core_ref, f32[8,32,256]{2,1,0:T(8,128)S(1)} %shard_map.98.near_ref, ...), custom_call_target="tpu_custom_call" | custom-call | tf_op jit(solution)/shard_map/pallas_call | solution.py:400
  79.2 3.3 %collective-permute-start.31 = (bf16[1,32,256]{2,1,0:T(8,128)(2,1)S(1)}, bf16[1,32,256]{2,1,0:T(8,128)(2,1)S(1)}, u32[]{:S(2)}, u32[]{:S(2)}) collective-permute-start(bf16[1,32,256]{2,1,0:T(8,128)(2,1)S(1)} %get-tuple-element.173), channel_id=1, source_target_pairs={{0,2},{1,3},{2,0},{3,1},{4,6},{5,7},{6,4},{7,5},{8,10},{9,11},{10,... | collective-permute-start | bytes 49160 | tf_op jit(solution)/shard_map/ppermute | solution.py:360
  82.5 1.8 %collective-permute-done.31.first_ref = bf16[1,32,256]{2,1,0:T(8,128)(2,1)S(1)} collective-permute-done((bf16[1,32,256]{2,1,0:T(8,128)(2,1)S(1)}, bf16[1,32,256]{2,1,0:T(8,128)(2,1)S(1)}, u32[]{:S(2)}, u32[]{:S(2)}) %collective-permute-start.31) | collective-permute-done | bytes 16416 | tf_op jit(solution)/shard_map/ppermute | solution.py:360
  84.3 3.9 %collective-permute-start.35 = (bf16[2,9,32,128]{3,2,1,0:T(8,128)(2,1)S(1)}, bf16[2,9,32,128]{3,2,1,0:T(8,128)(2,1)S(1)}, u32[]{:S(2)}, u32[]{:S(2)}) collective-permute-start(bf16[2,9,32,128]{3,2,1,0:T(8,128)(2,1)S(1)} %shard_map.106.refs_0_), channel_id=1, source_target_pairs={{0,8},{1,3},{2,10},{3,1},{4,12},{5,7},{6,14},{7,5},{8,0},{9,11},{1... | collective-permute-start | bytes 442376 | tf_op jit(solution)/shard_map/ppermute | solution.py:241
  88.2 1.6 %collective-permute-start.34 = (bf16[2,9,32,128]{3,2,1,0:T(8,128)(2,1)S(1)}, bf16[2,9,32,128]{3,2,1,0:T(8,128)(2,1)S(1)}, u32[]{:S(2)}, u32[]{:S(2)}) collective-permute-start(bf16[2,9,32,128]{3,2,1,0:T(8,128)(2,1)S(1)} %shard_map.106.refs_0_), channel_id=1, source_target_pairs={{0,4},{1,9},{2,6},{3,11},{4,0},{5,13},{6,2},{7,15},{8,12},{9,1},{1... | collective-permute-start | bytes 442376 | tf_op jit(solution)/shard_map/ppermute | solution.py:241
  89.8 1.1 collective-permute-start.33
  91.2 1.6 %collective-permute-done.35.refs_4_ = bf16[2,9,32,128]{3,2,1,0:T(8,128)(2,1)S(1)} collective-permute-done((bf16[2,9,32,128]{3,2,1,0:T(8,128)(2,1)S(1)}, bf16[2,9,32,128]{3,2,1,0:T(8,128)(2,1)S(1)}, u32[]{:S(2)}, u32[]{:S(2)}) %collective-permute-start.35) | collective-permute-done | bytes 147488 | tf_op jit(solution)/shard_map/ppermute | solution.py:241
  92.8 1.4 collective-permute-done.34.refs_2_
  94.2 0.8 collective-permute-done.33.refs_1_
  95.0 1.7 %collective-permute-start.36 = (bf16[2,9,32,128]{3,2,1,0:T(8,128)(2,1)S(1)}, bf16[2,9,32,128]{3,2,1,0:T(8,128)(2,1)S(1)}, u32[]{:S(2)}, u32[]{:S(2)}) collective-permute-start(bf16[2,9,32,128]{3,2,1,0:T(8,128)(2,1)S(1)} %collective-permute-done.33.refs_1_), channel_id=1, source_target_pairs={{0,4},{1,9},{2,6},{3,11},{4,0},{5,13},{6,2},{7,15},{8,12},{9,1},{1... | collective-permute-start | bytes 442376 | tf_op jit(solution)/shard_map/ppermute | solution.py:241
  96.7 1.1 collective-permute-start.38
  97.8 1.4 %collective-permute-start.37 = (bf16[2,9,32,128]{3,2,1,0:T(8,128)(2,1)S(1)}, bf16[2,9,32,128]{3,2,1,0:T(8,128)(2,1)S(1)}, u32[]{:S(2)}, u32[]{:S(2)}) collective-permute-start(bf16[2,9,32,128]{3,2,1,0:T(8,128)(2,1)S(1)} %collective-permute-done.35.refs_4_), channel_id=1, source_target_pairs={{0,2},{1,5},{2,0},{3,7},{4,6},{5,1},{6,4},{7,3},{8,10},{9,13},{10,... | collective-permute-start | bytes 442376 | tf_op jit(solution)/shard_map/ppermute | solution.py:241
  100.2 0.9 copy-done.12
  102.2 0.7 collective-permute-done.37.refs_5_
  105.0 3.9 %shard_map.108 = (bf16[4,2,9,32,128]{4,3,2,1,0:T(8,128)(2,1)S(1)}, bf16[4,2,9,32,128]{4,3,2,1,0:T(8,128)(2,1)S(1)}, bf16[4,2,9,32,128]{4,3,2,1,0:T(8,128)(2,1)S(1)}, bf16[4,2,9,32,128]{4,3,2,1,0:T(8,128)(2,1)S(1)}) custom-call(s32[128]{0:T(128)S(1)} %copy-done.19, s32[128]{0:T(128)S(1)} %copy-done.21, bf16[128,96,96]{2,1,0:T(8,128)(2,1)S(1)} %copy-done.4, ...), custom_call_target="tpu_custom_call" | custom-call | flops 75497472 | bytes 10485760 | tf_op jit(solution)/shard_map/pallas_call | solution.py:381
  109.3 1.7 %collective-permute-done.48.swap_ref = bf16[4,2,9,32,128]{4,3,2,1,0:T(8,128)(2,1)S(1)} collective-permute-done((bf16[4,2,9,32,128]{4,3,2,1,0:T(8,128)(2,1)S(1)}, bf16[4,2,9,32,128]{4,3,2,1,0:T(8,128)(2,1)S(1)}, u32[]{:S(2)}, u32[]{:S(2)}) %collective-permute-start.48) | collective-permute-done | bytes 589856 | tf_op jit(solution)/shard_map/ppermute | solution.py:246
  111.5 2.0 %collective-permute-start.49 = (bf16[2,9,32,128]{3,2,1,0:T(8,128)(2,1)S(1)}, bf16[2,9,32,128]{3,2,1,0:T(8,128)(2,1)S(1)}, u32[]{:S(2)}, u32[]{:S(2)}) collective-permute-start(bf16[2,9,32,128]{3,2,1,0:T(8,128)(2,1)S(1)} %get-tuple-element.196), channel_id=1, source_target_pairs={{0,4},{1,9},{2,6},{3,11},{4,0},{5,13},{6,2},{7,15},{8,12},{9,1},{1... | collective-permute-start | bytes 442376 | tf_op jit(solution)/shard_map/ppermute | solution.py:241
  113.7 2.0 %collective-permute-start.51 = (bf16[2,9,32,128]{3,2,1,0:T(8,128)(2,1)S(1)}, bf16[2,9,32,128]{3,2,1,0:T(8,128)(2,1)S(1)}, u32[]{:S(2)}, u32[]{:S(2)}) collective-permute-start(bf16[2,9,32,128]{3,2,1,0:T(8,128)(2,1)S(1)} %get-tuple-element.198), channel_id=1, source_target_pairs={{0,2},{1,5},{2,0},{3,7},{4,6},{5,1},{6,4},{7,3},{8,10},{9,13},{10,... | collective-permute-start | bytes 442376 | tf_op jit(solution)/shard_map/ppermute | solution.py:241
  115.7 1.0 collective-permute-start.56
  116.8 2.0 %collective-permute-done.50.refs_1_ = bf16[2,9,32,128]{3,2,1,0:T(8,128)(2,1)S(1)} collective-permute-done((bf16[2,9,32,128]{3,2,1,0:T(8,128)(2,1)S(1)}, bf16[2,9,32,128]{3,2,1,0:T(8,128)(2,1)S(1)}, u32[]{:S(2)}, u32[]{:S(2)}) %collective-permute-start.50) | collective-permute-done | bytes 147488 | tf_op jit(solution)/shard_map/ppermute | solution.py:241
  118.8 2.8 %collective-permute-done.51.refs_2_ = bf16[2,9,32,128]{3,2,1,0:T(8,128)(2,1)S(1)} collective-permute-done((bf16[2,9,32,128]{3,2,1,0:T(8,128)(2,1)S(1)}, bf16[2,9,32,128]{3,2,1,0:T(8,128)(2,1)S(1)}, u32[]{:S(2)}, u32[]{:S(2)}) %collective-permute-start.51) | collective-permute-done | bytes 147488 | tf_op jit(solution)/shard_map/ppermute | solution.py:241
  121.8 2.5 %collective-permute-start.53 = (bf16[2,9,32,128]{3,2,1,0:T(8,128)(2,1)S(1)}, bf16[2,9,32,128]{3,2,1,0:T(8,128)(2,1)S(1)}, u32[]{:S(2)}, u32[]{:S(2)}) collective-permute-start(bf16[2,9,32,128]{3,2,1,0:T(8,128)(2,1)S(1)} %get-tuple-element.212), channel_id=1, source_target_pairs={{0,2},{1,5},{2,0},{3,7},{4,6},{5,1},{6,4},{7,3},{8,10},{9,13},{10,... | collective-permute-start | bytes 442376 | tf_op jit(solution)/shard_map/ppermute | solution.py:241
  124.3 1.2 collective-permute-start.54
  125.5 0.9 collective-permute-start.55
  126.4 1.2 collective-permute-done.57.inner_ref
  127.7 1.0 collective-permute-done.58.outer_ref
  129.4 1.2 collective-permute-done.55.refs_2_
  130.7 0.9 collective-permute-start.59
  131.6 5.2 %collective-permute-done.59.rest_0_ = bf16[9,32,128]{2,1,0:T(8,128)(2,1)S(1)} collective-permute-done((bf16[9,32,128]{2,1,0:T(8,128)(2,1)S(1)}, bf16[9,32,128]{2,1,0:T(8,128)(2,1)S(1)}, u32[]{:S(2)}, u32[]{:S(2)}) %collective-permute-start.59) | collective-permute-done | bytes 73760 | tf_op jit(solution)/shard_map/ppermute | solution.py:237
  136.8 2.5 %shard_map.114 = bf16[8,32,256]{2,1,0:T(8,128)(2,1)} custom-call(s32[12]{0:T(128)S(1)} %copy-done.22, s32[1]{0:T(128)} %bitcast.core_ref, f32[8,32,256]{2,1,0:T(8,128)S(1)} %shard_map.107.near_ref, f32[2,32,256]{2,1,0:T(8,128)S(1)} %shard_map.112.edge_ref, bf16[8,96,256]{2,1,0:T(8,128)(2,1)S(1)} %copy-done.5, bf16[8,96,96]{2,1,0:T(8,128)(2,1)S(1)} %copy-done.6, ...), custom_call_target="tpu_custom_call" | custom-call | tf_op jit(solution)/shard_map/pallas_call | solution.py:400
  (128 shorter events, 14.3 us)
Async XLA Ops:
  3.5 12.4 %collective-permute-start = (bf16[9,32,128]{2,1,0:T(8,128)(2,1)}, bf16[9,32,128]{2,1,0:T(8,128)(2,1)S(1)}, u32[]{:S(2)}, u32[]{:S(2)}) collective-permute-start(bf16[9,32,128]{2,1,0:T(8,128)(2,1)} %get-tuple-element.115.refs_0_), channel_id=1, source_target_pairs={{0,16},{1,17},{2,18},{3,19},{4,20},{5,21},{6,22},{7,23},{8,24},{9,... | collective-permute-start | bytes 221192 | tf_op jit(solution)/shard_map/ppermute | solution.py:237
  14.3 21.1 %copy-start = (bf16[8,3,256,256]{3,2,1,0:T(8,128)(2,1)S(1)}, bf16[8,3,256,256]{3,2,1,0:T(8,128)(2,1)}, u32[]{:S(2)}) copy-start(bf16[8,3,256,256]{3,2,1,0:T(8,128)(2,1)} %last_ref.3) | copy-start | bytes 9437188
  16.0 13.0 %collective-permute-start.3 = (bf16[2,9,32,128]{3,2,1,0:T(8,128)(2,1)S(1)}, bf16[2,9,32,128]{3,2,1,0:T(8,128)(2,1)}, u32[]{:S(2)}, u32[]{:S(2)}) collective-permute-start(bf16[2,9,32,128]{3,2,1,0:T(8,128)(2,1)S(1)} %shard_map.97.refs_0_), channel_id=1, source_target_pairs={{0,8},{1,3},{2,10},{3,1},{4,12},{5,7},{6,14},{7,5},{8,0},{9,11},{1... | collective-permute-start | bytes 442376 | tf_op jit(solution)/shard_map/ppermute | solution.py:241
  17.6 11.4 %collective-permute-start.2 = (bf16[2,9,32,128]{3,2,1,0:T(8,128)(2,1)S(1)}, bf16[2,9,32,128]{3,2,1,0:T(8,128)(2,1)}, u32[]{:S(2)}, u32[]{:S(2)}) collective-permute-start(bf16[2,9,32,128]{3,2,1,0:T(8,128)(2,1)S(1)} %shard_map.97.refs_0_), channel_id=1, source_target_pairs={{0,4},{1,9},{2,6},{3,11},{4,0},{5,13},{6,2},{7,15},{8,12},{9,1},{1... | collective-permute-start | bytes 442376 | tf_op jit(solution)/shard_map/ppermute | solution.py:241
  19.1 9.9 %collective-permute-start.1 = (bf16[2,9,32,128]{3,2,1,0:T(8,128)(2,1)S(1)}, bf16[2,9,32,128]{3,2,1,0:T(8,128)(2,1)}, u32[]{:S(2)}, u32[]{:S(2)}) collective-permute-start(bf16[2,9,32,128]{3,2,1,0:T(8,128)(2,1)S(1)} %shard_map.97.refs_0_), channel_id=1, source_target_pairs={{0,2},{1,5},{2,0},{3,7},{4,6},{5,1},{6,4},{7,3},{8,10},{9,13},{10,... | collective-permute-start | bytes 442376 | tf_op jit(solution)/shard_map/ppermute | solution.py:241
  20.6 3.9 %collective-permute-start.5 = (bf16[1,32,256]{2,1,0:T(8,128)(2,1)S(1)}, bf16[1,32,256]{2,1,0:T(8,128)(2,1)S(1)}, u32[]{:S(2)}, u32[]{:S(2)}) collective-permute-start(bf16[1,32,256]{2,1,0:T(8,128)(2,1)S(1)} %copy-done.24), channel_id=1, source_target_pairs={{2,4},{3,5},{4,2},{5,3},{6,8},{7,9},{8,6},{9,7},{10,12},{11,13},{1... | collective-permute-start | bytes 49160 | tf_op jit(solution)/shard_map/ppermute | solution.py:360
  21.3 7.7 %collective-permute-start.4 = (bf16[1,32,256]{2,1,0:T(8,128)(2,1)S(1)}, bf16[1,32,256]{2,1,0:T(8,128)(2,1)S(1)}, u32[]{:S(2)}, u32[]{:S(2)}) collective-permute-start(bf16[1,32,256]{2,1,0:T(8,128)(2,1)S(1)} %copy-done.24), channel_id=1, source_target_pairs={{0,2},{1,3},{2,0},{3,1},{4,6},{5,7},{6,4},{7,5},{8,10},{9,11},{10,... | collective-permute-start | bytes 49160 | tf_op jit(solution)/shard_map/ppermute | solution.py:360
  25.1 8.1 %collective-permute-start.9 = (bf16[2,9,32,128]{3,2,1,0:T(8,128)(2,1)S(1)}, bf16[2,9,32,128]{3,2,1,0:T(8,128)(2,1)S(1)}, u32[]{:S(2)}, u32[]{:S(2)}) collective-permute-start(bf16[2,9,32,128]{3,2,1,0:T(8,128)(2,1)S(1)} %shard_map.97.refs_0_), channel_id=1, source_target_pairs={{0,14},{1,15},{2,12},{3,13},{4,10},{5,11},{6,8},{7,9},{8,6},{9,7},... | collective-permute-start | bytes 442376 | tf_op jit(solution)/shard_map/ppermute | solution.py:241
  29.0 6.4 %collective-permute-start.6 = (bf16[2,9,32,128]{3,2,1,0:T(8,128)(2,1)}, bf16[2,9,32,128]{3,2,1,0:T(8,128)(2,1)}, u32[]{:S(2)}, u32[]{:S(2)}) collective-permute-start(bf16[2,9,32,128]{3,2,1,0:T(8,128)(2,1)} %collective-permute-done.1.refs_1_), channel_id=1, source_target_pairs={{0,4},{1,9},{2,6},{3,11},{4,0},{5,13},{6,2},{7,15},{8,12},{9,1},{1... | collective-permute-start | bytes 442376 | tf_op jit(solution)/shard_map/ppermute | solution.py:241
  29.7 7.2 %collective-permute-start.8 = (bf16[2,9,32,128]{3,2,1,0:T(8,128)(2,1)}, bf16[2,9,32,128]{3,2,1,0:T(8,128)(2,1)}, u32[]{:S(2)}, u32[]{:S(2)}) collective-permute-start(bf16[2,9,32,128]{3,2,1,0:T(8,128)(2,1)} %collective-permute-done.2.refs_2_), channel_id=1, source_target_pairs={{0,8},{1,3},{2,10},{3,1},{4,12},{5,7},{6,14},{7,5},{8,0},{9,11},{1... | collective-permute-start | bytes 442376 | tf_op jit(solution)/shard_map/ppermute | solution.py:241
  31.3 6.2 %collective-permute-start.7 = (bf16[2,9,32,128]{3,2,1,0:T(8,128)(2,1)}, bf16[2,9,32,128]{3,2,1,0:T(8,128)(2,1)}, u32[]{:S(2)}, u32[]{:S(2)}) collective-permute-start(bf16[2,9,32,128]{3,2,1,0:T(8,128)(2,1)} %collective-permute-done.3.refs_4_), channel_id=1, source_target_pairs={{0,2},{1,5},{2,0},{3,7},{4,6},{5,1},{6,4},{7,3},{8,10},{9,13},{10,... | collective-permute-start | bytes 442376 | tf_op jit(solution)/shard_map/ppermute | solution.py:241
  32.1 5.5 %collective-permute-start.10 = (bf16[2,9,32,128]{3,2,1,0:T(8,128)(2,1)S(1)}, bf16[2,9,32,128]{3,2,1,0:T(8,128)(2,1)}, u32[]{:S(2)}, u32[]{:S(2)}) collective-permute-start(bf16[2,9,32,128]{3,2,1,0:T(8,128)(2,1)S(1)} %shard_map.97.refs_0_), channel_id=1, source_target_pairs={{0,1},{1,0},{2,3},{3,2},{4,5},{5,4},{6,7},{7,6},{8,9},{9,8},{10,11... | collective-permute-start | bytes 442376 | tf_op jit(solution)/shard_map/ppermute | solution.py:246
  33.2 4.8 %collective-permute-start.11 = (bf16[2,9,32,128]{3,2,1,0:T(8,128)(2,1)}, bf16[2,9,32,128]{3,2,1,0:T(8,128)(2,1)}, u32[]{:S(2)}, u32[]{:S(2)}) collective-permute-start(bf16[2,9,32,128]{3,2,1,0:T(8,128)(2,1)} %collective-permute-done.1.refs_1_), channel_id=1, source_target_pairs={{0,1},{1,0},{2,3},{3,2},{4,5},{5,4},{6,7},{7,6},{8,9},{9,8},{10,11... | collective-permute-start | bytes 442376 | tf_op jit(solution)/shard_map/ppermute | solution.py:246
  35.4 2.7 %collective-permute-start.12 = (bf16[2,9,32,128]{3,2,1,0:T(8,128)(2,1)}, bf16[2,9,32,128]{3,2,1,0:T(8,128)(2,1)}, u32[]{:S(2)}, u32[]{:S(2)}) collective-permute-start(bf16[2,9,32,128]{3,2,1,0:T(8,128)(2,1)} %collective-permute-done.2.refs_2_), channel_id=1, source_target_pairs={{0,1},{1,0},{2,3},{3,2},{4,5},{5,4},{6,7},{7,6},{8,9},{9,8},{10,11... | collective-permute-start | bytes 442376 | tf_op jit(solution)/shard_map/ppermute | solution.py:246
  36.9 2.3 %collective-permute-start.14 = (bf16[2,9,32,128]{3,2,1,0:T(8,128)(2,1)}, bf16[2,9,32,128]{3,2,1,0:T(8,128)(2,1)S(1)}, u32[]{:S(2)}, u32[]{:S(2)}) collective-permute-start(bf16[2,9,32,128]{3,2,1,0:T(8,128)(2,1)} %collective-permute-done.3.refs_4_), channel_id=1, source_target_pairs={{0,1},{1,0},{2,3},{3,2},{4,5},{5,4},{6,7},{7,6},{8,9},{9,8},{10,11... | collective-permute-start | bytes 442376 | tf_op jit(solution)/shard_map/ppermute | solution.py:246
  37.5 1.8 %collective-permute-start.13 = (bf16[2,9,32,128]{3,2,1,0:T(8,128)(2,1)}, bf16[2,9,32,128]{3,2,1,0:T(8,128)(2,1)S(1)}, u32[]{:S(2)}, u32[]{:S(2)}) collective-permute-start(bf16[2,9,32,128]{3,2,1,0:T(8,128)(2,1)} %collective-permute-done.6.refs_3_), channel_id=1, source_target_pairs={{0,1},{1,0},{2,3},{3,2},{4,5},{5,4},{6,7},{7,6},{8,9},{9,8},{10,11... | collective-permute-start | bytes 442376 | tf_op jit(solution)/shard_map/ppermute | solution.py:246
  37.6 1.7 %collective-permute-start.15 = (bf16[2,9,32,128]{3,2,1,0:T(8,128)(2,1)}, bf16[2,9,32,128]{3,2,1,0:T(8,128)(2,1)S(1)}, u32[]{:S(2)}, u32[]{:S(2)}) collective-permute-start(bf16[2,9,32,128]{3,2,1,0:T(8,128)(2,1)} %collective-permute-done.7.refs_5_), channel_id=1, source_target_pairs={{0,1},{1,0},{2,3},{3,2},{4,5},{5,4},{6,7},{7,6},{8,9},{9,8},{10,11... | collective-permute-start | bytes 442376 | tf_op jit(solution)/shard_map/ppermute | solution.py:246
  38.0 1.6 %collective-permute-start.16 = (bf16[2,9,32,128]{3,2,1,0:T(8,128)(2,1)}, bf16[2,9,32,128]{3,2,1,0:T(8,128)(2,1)S(1)}, u32[]{:S(2)}, u32[]{:S(2)}) collective-permute-start(bf16[2,9,32,128]{3,2,1,0:T(8,128)(2,1)} %collective-permute-done.8.refs_6_), channel_id=1, source_target_pairs={{0,1},{1,0},{2,3},{3,2},{4,5},{5,4},{6,7},{7,6},{8,9},{9,8},{10,11... | collective-permute-start | bytes 442376 | tf_op jit(solution)/shard_map/ppermute | solution.py:246
  38.1 1.5 %collective-permute-start.17 = (bf16[2,9,32,128]{3,2,1,0:T(8,128)(2,1)S(1)}, bf16[2,9,32,128]{3,2,1,0:T(8,128)(2,1)S(1)}, u32[]{:S(2)}, u32[]{:S(2)}) collective-permute-start(bf16[2,9,32,128]{3,2,1,0:T(8,128)(2,1)S(1)} %copy-done.11), channel_id=1, source_target_pairs={{0,1},{1,0},{2,3},{3,2},{4,5},{5,4},{6,7},{7,6},{8,9},{9,8},{10,11... | collective-permute-start | bytes 442376 | tf_op jit(solution)/shard_map/ppermute | solution.py:246
  45.9 2.0 %collective-permute-start.18 = (bf16[4,2,9,32,128]{4,3,2,1,0:T(8,128)(2,1)S(1)}, bf16[4,2,9,32,128]{4,3,2,1,0:T(8,128)(2,1)S(1)}, u32[]{:S(2)}, u32[]{:S(2)}) collective-permute-start(bf16[4,2,9,32,128]{4,3,2,1,0:T(8,128)(2,1)S(1)} %get-tuple-element.135), channel_id=1, source_target_pairs={{0,1},{1,0},{2,3},{3,2},{4,5},{5,4},{6,7},{7,6},{8,9},{9,8},{10,11... | collective-permute-start | bytes 1769480 | tf_op jit(solution)/shard_map/ppermute | solution.py:246
  49.4 8.9 %collective-permute-start.22 = (bf16[4,2,9,32,128]{4,3,2,1,0:T(8,128)(2,1)}, bf16[4,2,9,32,128]{4,3,2,1,0:T(8,128)(2,1)}, u32[]{:S(2)}, u32[]{:S(2)}) collective-permute-start(bf16[4,2,9,32,128]{4,3,2,1,0:T(8,128)(2,1)} %get-tuple-element.144), channel_id=1, source_target_pairs={{0,1},{1,0},{2,3},{3,2},{4,5},{5,4},{6,7},{7,6},{8,9},{9,8},{10,11... | collective-permute-start | bytes 1769480 | tf_op jit(solution)/shard_map/ppermute | solution.py:246
  49.7 6.7 %collective-permute-start.19 = (bf16[2,9,32,128]{3,2,1,0:T(8,128)(2,1)}, bf16[2,9,32,128]{3,2,1,0:T(8,128)(2,1)S(1)}, u32[]{:S(2)}, u32[]{:S(2)}) collective-permute-start(bf16[2,9,32,128]{3,2,1,0:T(8,128)(2,1)} %get-tuple-element.141), channel_id=1, source_target_pairs={{0,4},{1,9},{2,6},{3,11},{4,0},{5,13},{6,2},{7,15},{8,12},{9,1},{1... | collective-permute-start | bytes 442376 | tf_op jit(solution)/shard_map/ppermute | solution.py:241
  51.2 5.5 %collective-permute-start.20 = (bf16[2,9,32,128]{3,2,1,0:T(8,128)(2,1)}, bf16[2,9,32,128]{3,2,1,0:T(8,128)(2,1)}, u32[]{:S(2)}, u32[]{:S(2)}) collective-permute-start(bf16[2,9,32,128]{3,2,1,0:T(8,128)(2,1)} %get-tuple-element.142), channel_id=1, source_target_pairs={{0,8},{1,3},{2,10},{3,1},{4,12},{5,7},{6,14},{7,5},{8,0},{9,11},{1... | collective-permute-start | bytes 442376 | tf_op jit(solution)/shard_map/ppermute | solution.py:241
  52.8 5.5 %collective-permute-start.21 = (bf16[2,9,32,128]{3,2,1,0:T(8,128)(2,1)}, bf16[2,9,32,128]{3,2,1,0:T(8,128)(2,1)}, u32[]{:S(2)}, u32[]{:S(2)}) collective-permute-start(bf16[2,9,32,128]{3,2,1,0:T(8,128)(2,1)} %get-tuple-element.143), channel_id=1, source_target_pairs={{0,2},{1,5},{2,0},{3,7},{4,6},{5,1},{6,4},{7,3},{8,10},{9,13},{10,... | collective-permute-start | bytes 442376 | tf_op jit(solution)/shard_map/ppermute | solution.py:241
  54.5 13.5 %collective-permute-start.26 = (bf16[2,9,32,128]{3,2,1,0:T(8,128)(2,1)}, bf16[2,9,32,128]{3,2,1,0:T(8,128)(2,1)S(1)}, u32[]{:S(2)}, u32[]{:S(2)}) collective-permute-start(bf16[2,9,32,128]{3,2,1,0:T(8,128)(2,1)} %copy-done.23), channel_id=1, source_target_pairs={{0,14},{1,15},{2,12},{3,13},{4,10},{5,11},{6,8},{7,9},{8,6},{9,7},... | collective-permute-start | bytes 442376 | tf_op jit(solution)/shard_map/ppermute | solution.py:241
  60.7 7.3 %collective-permute-start.23 = (bf16[2,9,32,128]{3,2,1,0:T(8,128)(2,1)S(1)}, bf16[2,9,32,128]{3,2,1,0:T(8,128)(2,1)S(1)}, u32[]{:S(2)}, u32[]{:S(2)}) collective-permute-start(bf16[2,9,32,128]{3,2,1,0:T(8,128)(2,1)S(1)} %get-tuple-element.157), channel_id=1, source_target_pairs={{0,2},{1,5},{2,0},{3,7},{4,6},{5,1},{6,4},{7,3},{8,10},{9,13},{10,... | collective-permute-start | bytes 442376 | tf_op jit(solution)/shard_map/ppermute | solution.py:241
  61.1 7.3 %collective-permute-start.24 = (bf16[2,9,32,128]{3,2,1,0:T(8,128)(2,1)S(1)}, bf16[2,9,32,128]{3,2,1,0:T(8,128)(2,1)S(1)}, u32[]{:S(2)}, u32[]{:S(2)}) collective-permute-start(bf16[2,9,32,128]{3,2,1,0:T(8,128)(2,1)S(1)} %get-tuple-element.158), channel_id=1, source_target_pairs={{0,4},{1,9},{2,6},{3,11},{4,0},{5,13},{6,2},{7,15},{8,12},{9,1},{1... | collective-permute-start | bytes 442376 | tf_op jit(solution)/shard_map/ppermute | solution.py:241
  65.3 5.1 %collective-permute-start.25 = (bf16[2,9,32,128]{3,2,1,0:T(8,128)(2,1)S(1)}, bf16[2,9,32,128]{3,2,1,0:T(8,128)(2,1)S(1)}, u32[]{:S(2)}, u32[]{:S(2)}) collective-permute-start(bf16[2,9,32,128]{3,2,1,0:T(8,128)(2,1)S(1)} %get-tuple-element.159), channel_id=1, source_target_pairs={{0,8},{1,3},{2,10},{3,1},{4,12},{5,7},{6,14},{7,5},{8,0},{9,11},{1... | collective-permute-start | bytes 442376 | tf_op jit(solution)/shard_map/ppermute | solution.py:241
  65.3 1.4 %collective-permute-start.27 = (bf16[1,32,256]{2,1,0:T(8,128)(2,1)}, bf16[1,32,256]{2,1,0:T(8,128)(2,1)S(1)}, u32[]{:S(2)}, u32[]{:S(2)}) collective-permute-start(bf16[1,32,256]{2,1,0:T(8,128)(2,1)} %get-tuple-element.161), channel_id=1, source_target_pairs={{0,1},{1,0},{2,3},{3,2},{4,5},{5,4},{6,7},{7,6},{8,9},{9,8},{10,11... | collective-permute-start | bytes 49160 | tf_op jit(solution)/shard_map/ppermute | solution.py:246
  66.7 1.2 collective-permute-start.28
  67.9 37.1 %copy-start.19 = (s32[128]{0:T(128)S(1)}, s32[128]{0:T(128)}, u32[]{:S(2)}) copy-start(s32[128]{0:T(128)} %copy-done.18) | copy-start | bytes 1540
  67.9 37.1 %copy-start.21 = (s32[128]{0:T(128)S(1)}, s32[128]{0:T(128)}, u32[]{:S(2)}) copy-start(s32[128]{0:T(128)} %copy-done.20) | copy-start | bytes 1540
  68.0 37.0 %copy-start.4 = (bf16[128,96,96]{2,1,0:T(8,128)(2,1)S(1)}, bf16[128,96,96]{2,1,0:T(8,128)(2,1)}, u32[]{:S(2)}) copy-start(bf16[128,96,96]{2,1,0:T(8,128)(2,1)} %copy-done.2) | copy-start | bytes 7077892
  70.5 5.5 %collective-permute-start.29 = (bf16[9,32,128]{2,1,0:T(8,128)(2,1)S(1)}, bf16[9,32,128]{2,1,0:T(8,128)(2,1)S(1)}, u32[]{:S(2)}, u32[]{:S(2)}) collective-permute-start(bf16[9,32,128]{2,1,0:T(8,128)(2,1)S(1)} %get-tuple-element.170), channel_id=1, source_target_pairs={{0,16},{1,17},{2,18},{3,19},{4,20},{5,21},{6,22},{7,23},{8,24},{9,... | collective-permute-start | bytes 221192 | tf_op jit(solution)/shard_map/ppermute | solution.py:237
  78.6 5.7 %collective-permute-start.30 = (bf16[9,32,128]{2,1,0:T(8,128)(2,1)S(1)}, bf16[9,32,128]{2,1,0:T(8,128)(2,1)S(1)}, u32[]{:S(2)}, u32[]{:S(2)}) collective-permute-start(bf16[9,32,128]{2,1,0:T(8,128)(2,1)S(1)} %get-tuple-element.172.refs_0_), channel_id=1, source_target_pairs={{0,16},{1,17},{2,18},{3,19},{4,20},{5,21},{6,22},{7,23},{8,24},{9,... | collective-permute-start | bytes 221192 | tf_op jit(solution)/shard_map/ppermute | solution.py:237
  78.6 3.9 %collective-permute-start.32 = (bf16[1,32,256]{2,1,0:T(8,128)(2,1)S(1)}, bf16[1,32,256]{2,1,0:T(8,128)(2,1)S(1)}, u32[]{:S(2)}, u32[]{:S(2)}) collective-permute-start(bf16[1,32,256]{2,1,0:T(8,128)(2,1)S(1)} %get-tuple-element.173), channel_id=1, source_target_pairs={{2,4},{3,5},{4,2},{5,3},{6,8},{7,9},{8,6},{9,7},{10,12},{11,13},{1... | collective-permute-start | bytes 49160 | tf_op jit(solution)/shard_map/ppermute | solution.py:360
  79.2 5.1 %collective-permute-start.31 = (bf16[1,32,256]{2,1,0:T(8,128)(2,1)S(1)}, bf16[1,32,256]{2,1,0:T(8,128)(2,1)S(1)}, u32[]{:S(2)}, u32[]{:S(2)}) collective-permute-start(bf16[1,32,256]{2,1,0:T(8,128)(2,1)S(1)} %get-tuple-element.173), channel_id=1, source_target_pairs={{0,2},{1,3},{2,0},{3,1},{4,6},{5,7},{6,4},{7,5},{8,10},{9,11},{10,... | collective-permute-start | bytes 49160 | tf_op jit(solution)/shard_map/ppermute | solution.py:360
  84.3 8.5 %collective-permute-start.35 = (bf16[2,9,32,128]{3,2,1,0:T(8,128)(2,1)S(1)}, bf16[2,9,32,128]{3,2,1,0:T(8,128)(2,1)S(1)}, u32[]{:S(2)}, u32[]{:S(2)}) collective-permute-start(bf16[2,9,32,128]{3,2,1,0:T(8,128)(2,1)S(1)} %shard_map.106.refs_0_), channel_id=1, source_target_pairs={{0,8},{1,3},{2,10},{3,1},{4,12},{5,7},{6,14},{7,5},{8,0},{9,11},{1... | collective-permute-start | bytes 442376 | tf_op jit(solution)/shard_map/ppermute | solution.py:241
  88.2 6.0 %collective-permute-start.34 = (bf16[2,9,32,128]{3,2,1,0:T(8,128)(2,1)S(1)}, bf16[2,9,32,128]{3,2,1,0:T(8,128)(2,1)S(1)}, u32[]{:S(2)}, u32[]{:S(2)}) collective-permute-start(bf16[2,9,32,128]{3,2,1,0:T(8,128)(2,1)S(1)} %shard_map.106.refs_0_), channel_id=1, source_target_pairs={{0,4},{1,9},{2,6},{3,11},{4,0},{5,13},{6,2},{7,15},{8,12},{9,1},{1... | collective-permute-start | bytes 442376 | tf_op jit(solution)/shard_map/ppermute | solution.py:241
  89.8 5.2 %collective-permute-start.33 = (bf16[2,9,32,128]{3,2,1,0:T(8,128)(2,1)S(1)}, bf16[2,9,32,128]{3,2,1,0:T(8,128)(2,1)S(1)}, u32[]{:S(2)}, u32[]{:S(2)}) collective-permute-start(bf16[2,9,32,128]{3,2,1,0:T(8,128)(2,1)S(1)} %shard_map.106.refs_0_), channel_id=1, source_target_pairs={{0,2},{1,5},{2,0},{3,7},{4,6},{5,1},{6,4},{7,3},{8,10},{9,13},{10,... | collective-permute-start | bytes 442376 | tf_op jit(solution)/shard_map/ppermute | solution.py:241
  90.9 8.3 %collective-permute-start.39 = (bf16[2,9,32,128]{3,2,1,0:T(8,128)(2,1)S(1)}, bf16[2,9,32,128]{3,2,1,0:T(8,128)(2,1)S(1)}, u32[]{:S(2)}, u32[]{:S(2)}) collective-permute-start(bf16[2,9,32,128]{3,2,1,0:T(8,128)(2,1)S(1)} %shard_map.106.refs_0_), channel_id=1, source_target_pairs={{0,14},{1,15},{2,12},{3,13},{4,10},{5,11},{6,8},{7,9},{8,6},{9,7},... | collective-permute-start | bytes 442376 | tf_op jit(solution)/shard_map/ppermute | solution.py:241
  95.0 5.1 %collective-permute-start.36 = (bf16[2,9,32,128]{3,2,1,0:T(8,128)(2,1)S(1)}, bf16[2,9,32,128]{3,2,1,0:T(8,128)(2,1)S(1)}, u32[]{:S(2)}, u32[]{:S(2)}) collective-permute-start(bf16[2,9,32,128]{3,2,1,0:T(8,128)(2,1)S(1)} %collective-permute-done.33.refs_1_), channel_id=1, source_target_pairs={{0,4},{1,9},{2,6},{3,11},{4,0},{5,13},{6,2},{7,15},{8,12},{9,1},{1... | collective-permute-start | bytes 442376 | tf_op jit(solution)/shard_map/ppermute | solution.py:241
  96.7 5.1 %collective-permute-start.38 = (bf16[2,9,32,128]{3,2,1,0:T(8,128)(2,1)S(1)}, bf16[2,9,32,128]{3,2,1,0:T(8,128)(2,1)S(1)}, u32[]{:S(2)}, u32[]{:S(2)}) collective-permute-start(bf16[2,9,32,128]{3,2,1,0:T(8,128)(2,1)S(1)} %collective-permute-done.34.refs_2_), channel_id=1, source_target_pairs={{0,8},{1,3},{2,10},{3,1},{4,12},{5,7},{6,14},{7,5},{8,0},{9,11},{1... | collective-permute-start | bytes 442376 | tf_op jit(solution)/shard_map/ppermute | solution.py:241
  97.8 5.1 %collective-permute-start.37 = (bf16[2,9,32,128]{3,2,1,0:T(8,128)(2,1)S(1)}, bf16[2,9,32,128]{3,2,1,0:T(8,128)(2,1)S(1)}, u32[]{:S(2)}, u32[]{:S(2)}) collective-permute-start(bf16[2,9,32,128]{3,2,1,0:T(8,128)(2,1)S(1)} %collective-permute-done.35.refs_4_), channel_id=1, source_target_pairs={{0,2},{1,5},{2,0},{3,7},{4,6},{5,1},{6,4},{7,3},{8,10},{9,13},{10,... | collective-permute-start | bytes 442376 | tf_op jit(solution)/shard_map/ppermute | solution.py:241
  99.2 3.7 %collective-permute-start.40 = (bf16[2,9,32,128]{3,2,1,0:T(8,128)(2,1)S(1)}, bf16[2,9,32,128]{3,2,1,0:T(8,128)(2,1)S(1)}, u32[]{:S(2)}, u32[]{:S(2)}) collective-permute-start(bf16[2,9,32,128]{3,2,1,0:T(8,128)(2,1)S(1)} %shard_map.106.refs_0_), channel_id=1, source_target_pairs={{0,1},{1,0},{2,3},{3,2},{4,5},{5,4},{6,7},{7,6},{8,9},{9,8},{10,11... | collective-permute-start | bytes 442376 | tf_op jit(solution)/shard_map/ppermute | solution.py:246
  99.2 4.2 %collective-permute-start.41 = (bf16[2,9,32,128]{3,2,1,0:T(8,128)(2,1)S(1)}, bf16[2,9,32,128]{3,2,1,0:T(8,128)(2,1)S(1)}, u32[]{:S(2)}, u32[]{:S(2)}) collective-permute-start(bf16[2,9,32,128]{3,2,1,0:T(8,128)(2,1)S(1)} %collective-permute-done.33.refs_1_), channel_id=1, source_target_pairs={{0,1},{1,0},{2,3},{3,2},{4,5},{5,4},{6,7},{7,6},{8,9},{9,8},{10,11... | collective-permute-start | bytes 442376 | tf_op jit(solution)/shard_map/ppermute | solution.py:246
  100.2 3.3 %collective-permute-start.42 = (bf16[2,9,32,128]{3,2,1,0:T(8,128)(2,1)S(1)}, bf16[2,9,32,128]{3,2,1,0:T(8,128)(2,1)S(1)}, u32[]{:S(2)}, u32[]{:S(2)}) collective-permute-start(bf16[2,9,32,128]{3,2,1,0:T(8,128)(2,1)S(1)} %collective-permute-done.34.refs_2_), channel_id=1, source_target_pairs={{0,1},{1,0},{2,3},{3,2},{4,5},{5,4},{6,7},{7,6},{8,9},{9,8},{10,11... | collective-permute-start | bytes 442376 | tf_op jit(solution)/shard_map/ppermute | solution.py:246
  101.8 2.1 %collective-permute-start.44 = (bf16[2,9,32,128]{3,2,1,0:T(8,128)(2,1)S(1)}, bf16[2,9,32,128]{3,2,1,0:T(8,128)(2,1)S(1)}, u32[]{:S(2)}, u32[]{:S(2)}) collective-permute-start(bf16[2,9,32,128]{3,2,1,0:T(8,128)(2,1)S(1)} %collective-permute-done.35.refs_4_), channel_id=1, source_target_pairs={{0,1},{1,0},{2,3},{3,2},{4,5},{5,4},{6,7},{7,6},{8,9},{9,8},{10,11... | collective-permute-start | bytes 442376 | tf_op jit(solution)/shard_map/ppermute | solution.py:246
  102.9 1.4 collective-permute-start.43
  102.9 1.6 %collective-permute-start.45 = (bf16[2,9,32,128]{3,2,1,0:T(8,128)(2,1)S(1)}, bf16[2,9,32,128]{3,2,1,0:T(8,128)(2,1)S(1)}, u32[]{:S(2)}, u32[]{:S(2)}) collective-permute-start(bf16[2,9,32,128]{3,2,1,0:T(8,128)(2,1)S(1)} %collective-permute-done.37.refs_5_), channel_id=1, source_target_pairs={{0,1},{1,0},{2,3},{3,2},{4,5},{5,4},{6,7},{7,6},{8,9},{9,8},{10,11... | collective-permute-start | bytes 442376 | tf_op jit(solution)/shard_map/ppermute | solution.py:246
  103.4 1.4 collective-permute-start.46
  103.5 1.5 %collective-permute-start.47 = (bf16[2,9,32,128]{3,2,1,0:T(8,128)(2,1)S(1)}, bf16[2,9,32,128]{3,2,1,0:T(8,128)(2,1)S(1)}, u32[]{:S(2)}, u32[]{:S(2)}) collective-permute-start(bf16[2,9,32,128]{3,2,1,0:T(8,128)(2,1)S(1)} %collective-permute-done.39.refs_7_), channel_id=1, source_target_pairs={{0,1},{1,0},{2,3},{3,2},{4,5},{5,4},{6,7},{7,6},{8,9},{9,8},{10,11... | collective-permute-start | bytes 442376 | tf_op jit(solution)/shard_map/ppermute | solution.py:246
  108.9 2.1 %collective-permute-start.48 = (bf16[4,2,9,32,128]{4,3,2,1,0:T(8,128)(2,1)S(1)}, bf16[4,2,9,32,128]{4,3,2,1,0:T(8,128)(2,1)S(1)}, u32[]{:S(2)}, u32[]{:S(2)}) collective-permute-start(bf16[4,2,9,32,128]{4,3,2,1,0:T(8,128)(2,1)S(1)} %get-tuple-element.190), channel_id=1, source_target_pairs={{0,1},{1,0},{2,3},{3,2},{4,5},{5,4},{6,7},{7,6},{8,9},{9,8},{10,11... | collective-permute-start | bytes 1769480 | tf_op jit(solution)/shard_map/ppermute | solution.py:246
  111.1 10.5 %collective-permute-start.52 = (bf16[4,2,9,32,128]{4,3,2,1,0:T(8,128)(2,1)S(1)}, bf16[4,2,9,32,128]{4,3,2,1,0:T(8,128)(2,1)S(1)}, u32[]{:S(2)}, u32[]{:S(2)}) collective-permute-start(bf16[4,2,9,32,128]{4,3,2,1,0:T(8,128)(2,1)S(1)} %get-tuple-element.199), channel_id=1, source_target_pairs={{0,1},{1,0},{2,3},{3,2},{4,5},{5,4},{6,7},{7,6},{8,9},{9,8},{10,11... | collective-permute-start | bytes 1769480 | tf_op jit(solution)/shard_map/ppermute | solution.py:246
  111.5 5.4 %collective-permute-start.49 = (bf16[2,9,32,128]{3,2,1,0:T(8,128)(2,1)S(1)}, bf16[2,9,32,128]{3,2,1,0:T(8,128)(2,1)S(1)}, u32[]{:S(2)}, u32[]{:S(2)}) collective-permute-start(bf16[2,9,32,128]{3,2,1,0:T(8,128)(2,1)S(1)} %get-tuple-element.196), channel_id=1, source_target_pairs={{0,4},{1,9},{2,6},{3,11},{4,0},{5,13},{6,2},{7,15},{8,12},{9,1},{1... | collective-permute-start | bytes 442376 | tf_op jit(solution)/shard_map/ppermute | solution.py:241
  113.5 5.3 %collective-permute-start.50 = (bf16[2,9,32,128]{3,2,1,0:T(8,128)(2,1)S(1)}, bf16[2,9,32,128]{3,2,1,0:T(8,128)(2,1)S(1)}, u32[]{:S(2)}, u32[]{:S(2)}) collective-permute-start(bf16[2,9,32,128]{3,2,1,0:T(8,128)(2,1)S(1)} %get-tuple-element.197), channel_id=1, source_target_pairs={{0,8},{1,3},{2,10},{3,1},{4,12},{5,7},{6,14},{7,5},{8,0},{9,11},{1... | collective-permute-start | bytes 442376 | tf_op jit(solution)/shard_map/ppermute | solution.py:241
  113.7 7.8 %collective-permute-start.51 = (bf16[2,9,32,128]{3,2,1,0:T(8,128)(2,1)S(1)}, bf16[2,9,32,128]{3,2,1,0:T(8,128)(2,1)S(1)}, u32[]{:S(2)}, u32[]{:S(2)}) collective-permute-start(bf16[2,9,32,128]{3,2,1,0:T(8,128)(2,1)S(1)} %get-tuple-element.198), channel_id=1, source_target_pairs={{0,2},{1,5},{2,0},{3,7},{4,6},{5,1},{6,4},{7,3},{8,10},{9,13},{10,... | collective-permute-start | bytes 442376 | tf_op jit(solution)/shard_map/ppermute | solution.py:241
  115.7 13.2 %collective-permute-start.56 = (bf16[2,9,32,128]{3,2,1,0:T(8,128)(2,1)S(1)}, bf16[2,9,32,128]{3,2,1,0:T(8,128)(2,1)S(1)}, u32[]{:S(2)}, u32[]{:S(2)}) collective-permute-start(bf16[2,9,32,128]{3,2,1,0:T(8,128)(2,1)S(1)} %get-tuple-element.215), channel_id=1, source_target_pairs={{0,14},{1,15},{2,12},{3,13},{4,10},{5,11},{6,8},{7,9},{8,6},{9,7},... | collective-permute-start | bytes 442376 | tf_op jit(solution)/shard_map/ppermute | solution.py:241
  121.8 7.2 %collective-permute-start.53 = (bf16[2,9,32,128]{3,2,1,0:T(8,128)(2,1)S(1)}, bf16[2,9,32,128]{3,2,1,0:T(8,128)(2,1)S(1)}, u32[]{:S(2)}, u32[]{:S(2)}) collective-permute-start(bf16[2,9,32,128]{3,2,1,0:T(8,128)(2,1)S(1)} %get-tuple-element.212), channel_id=1, source_target_pairs={{0,2},{1,5},{2,0},{3,7},{4,6},{5,1},{6,4},{7,3},{8,10},{9,13},{10,... | collective-permute-start | bytes 442376 | tf_op jit(solution)/shard_map/ppermute | solution.py:241
  124.3 5.1 %collective-permute-start.54 = (bf16[2,9,32,128]{3,2,1,0:T(8,128)(2,1)S(1)}, bf16[2,9,32,128]{3,2,1,0:T(8,128)(2,1)S(1)}, u32[]{:S(2)}, u32[]{:S(2)}) collective-permute-start(bf16[2,9,32,128]{3,2,1,0:T(8,128)(2,1)S(1)} %get-tuple-element.213), channel_id=1, source_target_pairs={{0,4},{1,9},{2,6},{3,11},{4,0},{5,13},{6,2},{7,15},{8,12},{9,1},{1... | collective-permute-start | bytes 442376 | tf_op jit(solution)/shard_map/ppermute | solution.py:241
  125.5 5.1 %collective-permute-start.55 = (bf16[2,9,32,128]{3,2,1,0:T(8,128)(2,1)S(1)}, bf16[2,9,32,128]{3,2,1,0:T(8,128)(2,1)S(1)}, u32[]{:S(2)}, u32[]{:S(2)}) collective-permute-start(bf16[2,9,32,128]{3,2,1,0:T(8,128)(2,1)S(1)} %get-tuple-element.214), channel_id=1, source_target_pairs={{0,8},{1,3},{2,10},{3,1},{4,12},{5,7},{6,14},{7,5},{8,0},{9,11},{1... | collective-permute-start | bytes 442376 | tf_op jit(solution)/shard_map/ppermute | solution.py:241
  126.4 1.2 collective-permute-start.57
  127.6 1.2 collective-permute-start.58
  130.7 6.1 %collective-permute-start.59 = (bf16[9,32,128]{2,1,0:T(8,128)(2,1)S(1)}, bf16[9,32,128]{2,1,0:T(8,128)(2,1)S(1)}, u32[]{:S(2)}, u32[]{:S(2)}) collective-permute-start(bf16[9,32,128]{2,1,0:T(8,128)(2,1)S(1)} %get-tuple-element.225), channel_id=1, source_target_pairs={{0,16},{1,17},{2,18},{3,19},{4,20},{5,21},{6,22},{7,23},{8,24},{9,... | collective-permute-start | bytes 221192 | tf_op jit(solution)/shard_map/ppermute | solution.py:237
  (21 other events, 96.5 us)

commit v13 on v12

--- a/solution.py
+++ b/solution.py
@@ -133,7 +133,7 @@
     lax.fori_loop(0, far, pack, 0)
 
 
-def near_kernel(v_ref, near_ref, out_ref):
+def near_kernel(v_ref, near_ref, _, out_ref):
     leaves = v_ref.shape[0]
     for i in range(leaves):
         total = dot(v_ref[i], near_ref[i, 1])
@@ -280,7 +280,7 @@
 
     order = ((x | y | z, x | y, y | z, z | x), (0, x, y, z))
     couple = pl.pallas_call(
-        functools.partial(couple_kernel, order=order, unroll=32),
+        functools.partial(couple_kernel, order=order, unroll=64),
         out_shape=[shape((4, far) + tile_shape, BF)] * 4,
         in_specs=[SMEM, SMEM, VMEM] + [VMEM] * (cores * chips),
         out_specs=[VMEM] * 4,
@@ -288,7 +288,7 @@
             pltpu.VMEM((devices * clusters, rhs, LANES), BF),
             pltpu.VMEM((devices * clusters, rhs, LANES), F32),
         ],
-        compiler_params=params(32 if devices <= 32 else 60),
+        compiler_params=params(24 if devices <= 32 else 60),
         cost_estimate=pl.CostEstimate(
             flops=2 * blocks * rhs * rank_top * rank_top, bytes_accessed=10 << 20, transcendentals=0
         ),
@@ -297,7 +297,7 @@
     near = pl.pallas_call(
         near_kernel,
         out_shape=shape((leaves, rhs, width), F32),
-        in_specs=[VMEM] * 2,
+        in_specs=[VMEM, VMEM, pl.BlockSpec(memory_space=pl.ANY)],
         out_specs=VMEM,
         compiler_params=params(16),
         cost_estimate=pl.CostEstimate(
@@ -360,33 +360,26 @@
         return [lax.ppermute(edge_row, "clu", pairs) for pairs in halo_pairs]
 
     def apply_matrix(field_in, coeffs, inner, outer, coupling, with_coeffs):
-        away = [swap_far(coeffs, s) for s in range(1, far)]
-        if with_coeffs:
-            away, coupling = barrier((away, coupling))
-        else:
-            away, outer = barrier((away, swap_halo(outer)))
-        (column,) = join(coeffs, *away)
+        (column,) = join(coeffs, *[swap_far(coeffs, s) for s in range(1, far)])
         got = {0: column, x: swap(column, x), y: swap(column, y), z: swap(column, z)}
-        if with_coeffs:
-            got, outer = barrier((got, swap_halo(outer)))
-        else:
-            got = barrier(got)
+        near_sum = near(field_in, near_field, coupling)
+        got, near_sum = barrier((got, near_sum))
         corner = swap(column, x | y | z)
         other = {chip: swap_cores(part) for chip, part in got.items()}
         got |= {x | y: swap(got[x], y), y | z: swap(got[y], z), z | x: swap(got[z], x)}
-        near_sum = near(field_in, near_field)
-        got, corner, near_sum = barrier((got, corner, near_sum))
+        got, corner = barrier((got, corner))
         got[x | y | z] = corner
         other |= {chip: swap_cores(got[chip]) for chip in order[0]}
-        keep_long, keep, send_long, send = couple(
+        totals = couple(
             source_rows,
             target_rows,
             coupling,
             *[got[chip] for chip in range(chips)],
             *[other[chip] for chip in range(chips)],
         )
+        (keep_long, keep, send_long, send), outer = barrier((totals, outer))
         corner, xy, yz, zx = far_add(keep_long, swap_cores(send_long))
-        corner, xy, yz, zx, send = barrier((corner, xy, yz, zx, send))
+        corner, xy, yz, zx, send, outer = barrier((corner, xy, yz, zx, send, swap_halo(outer)))
         to_x, to_y, to_z, swapped = barrier((swap(xy, y), swap(yz, z), swap(zx, x), swap_cores(send)))
         own, to_x, to_y, to_z, inner, outer = barrier(
             (*middle_add(keep, swapped, to_x, to_y, to_z), inner, pick(halo_turn, *outer))
@@ -399,15 +392,6 @@
         terms = [swap_far(part, s + 1) for s, part in enumerate(away)]
         return finish(with_coeffs)(ranks, core_index, near_sum, edges, basis, transfer, total, *terms)
 
-    coupling, first_coeffs = barrier((coupling, first_coeffs))
-    coupling = pl.pallas_call(
-        lambda in_ref, out_ref: None,
-        out_shape=shape(coupling.shape, BF),
-        in_specs=[pl.BlockSpec(memory_space=pl.ANY)],
-        out_specs=pl.BlockSpec(memory_space=pl.ANY),
-        input_output_aliases={0: 0},
-        compiler_params=params(1),
-    )(coupling)
     first, *second_args = apply_matrix(charges, first_coeffs, inner, outer, coupling, True)
     (second,) = apply_matrix(first, *second_args, coupling, False)
     return (first, second)

time: 140 us -> 149 us (1.064)
  waiting for transfers between devices: 41 us -> 53 us
  starting transfers between devices: 60.5 us -> 54.2 us
  local copies, waits for them, and re-layouts: 14.7 us -> 18.1 us
    unnamed x50 -> x49, local copies, waits for them, and re-layouts: 9.95 us -> 18.1 us
    ppermute x4, waiting for transfers between devices: 10.7 us -> 18.6 us  [swap_far(): lax.ppermute(part, 'clu', [(d, (d + shift * cube) % devices) for d in ran...]
    ppermute x28, starting transfers between devices: 42.3 us -> 35 us  [swap(): lax.ppermute(part, 'clu', [(d, d ^ (turned if d % cores else direction) *...]
    ppermute x28, waiting for transfers between devices: 19.2 us -> 25.7 us  [swap(): lax.ppermute(part, 'clu', [(d, d ^ (turned if d % cores else direction) *...]
    optimization_barrier x1 -> x0, local copies, waits for them, and re-layouts: 4.76 us -> none  [local(): coupling, first_coeffs = barrier((coupling, first_coeffs))]
    ppermute x24, waiting for transfers between devices: 9.4 us -> 7.11 us  [swap_cores(): return lax.ppermute(part, 'clu', [(d, d ^ 1) for d in range(devices)])]
    ppermute x4, starting transfers between devices: 5.07 us -> 6.83 us  [swap_far(): lax.ppermute(part, 'clu', [(d, (d + shift * cube) % devices) for d in ran...]
    ppermute x24, starting transfers between devices: 5.21 us -> 3.63 us  [swap_cores(): return lax.ppermute(part, 'clu', [(d, d ^ 1) for d in range(devices)])]
  transfers between devices with their start and end apart: 60 -> 60, of which waited for: 31 -> 33; matrix products, arithmetic and copies ran while one was open for 4% -> 4% of each run, Pallas kernels for 2% -> 3%
where the time goes in v13:
time: 149 us; the launch traced here: 148 us
  starting transfers between devices  54.2 us (36%)
  waiting for transfers between devices  53 us (36%)
  Pallas kernels  21.2 us (14%)
  local copies, waits for them, and re-layouts  18.1 us (12%)
    ppermute x28, starting transfers between devices, swap(): lax.ppermute(part, 'clu', [(d, d ^ (turned if d % cores else direction) *...  35 us
    ppermute x28, waiting for transfers between devices, swap(): lax.ppermute(part, 'clu', [(d, d ^ (turned if d % cores else direction) *...  25.7 us
    ppermute x4, waiting for transfers between devices, swap_far(): lax.ppermute(part, 'clu', [(d, (d + shift * cube) % devices) for d in ran...  18.6 us
    unnamed x49, local copies, waits for them, and re-layouts  18.1 us
    pallas_call x2, Pallas kernels, apply_matrix(): couple(source_rows, target_rows, coupling, *[got[chip] for chip in range(...  8.92 us
    ppermute x4, starting transfers between devices, swap_halo(): return [lax.ppermute(edge_row, 'clu', pairs) for pairs in halo_pairs]  8.75 us
    ppermute x24, waiting for transfers between devices, swap_cores(): return lax.ppermute(part, 'clu', [(d, d ^ 1) for d in range(devices)])  7.11 us
    ppermute x4, starting transfers between devices, swap_far(): lax.ppermute(part, 'clu', [(d, (d + shift * cube) % devices) for d in ran...  6.83 us
  transfers between devices with their start and end apart: 60, of which 33 were waited for; matrix products, arithmetic and copies ran while one was open for 4% of the time, Pallas kernels for 3%

profile of v13, /device:TPU:0, one launch (start us, length us, event | category | flops | bytes accessed | tf_op | source)
XLA Modules:
  0.0 148.1 jit_solution(6121087381909113064)
XLA Ops:
  0.7 3.2 %shard_map.95 = (bf16[9,32,128]{2,1,0:T(8,128)(2,1)}, bf16[1,32,256]{2,1,0:T(8,128)(2,1)}, bf16[1,32,256]{2,1,0:T(8,128)(2,1)}) custom-call(s32[12]{0:T(128)} %ranks_ref.5, s32[1]{0:T(128)} %bitcast.core_ref, bf16[8,32,256]{2,1,0:T(8,128)(2,1)} %v_ref.1, bf16[8,96,256]{2,1,0:T(8,128)(2,1)} %basis_ref.3, bf16[8,96,96]{2,1,0:T(8,128)(2,1)} %transfer_ref.3), custom_call_target="tpu_custom_call" | custom-call | tf_op jit(solution)/shard_map/pallas_call | solution.py:268
  3.8 4.1 %collective-permute-start = (bf16[9,32,128]{2,1,0:T(8,128)(2,1)}, bf16[9,32,128]{2,1,0:T(8,128)(2,1)S(1)}, u32[]{:S(2)}, u32[]{:S(2)}) collective-permute-start(bf16[9,32,128]{2,1,0:T(8,128)(2,1)} %get-tuple-element.119.refs_0_), channel_id=1, source_target_pairs={{0,16},{1,17},{2,18},{3,19},{4,20},{5,21},{6,22},{7,23},{8,24},{9,... | collective-permute-start | bytes 221192 | tf_op jit(solution)/shard_map/ppermute | solution.py:237
  7.9 4.1 %collective-permute-done.refs_1_ = bf16[9,32,128]{2,1,0:T(8,128)(2,1)S(1)} collective-permute-done((bf16[9,32,128]{2,1,0:T(8,128)(2,1)}, bf16[9,32,128]{2,1,0:T(8,128)(2,1)S(1)}, u32[]{:S(2)}, u32[]{:S(2)}) %collective-permute-start) | collective-permute-done | bytes 73760 | tf_op jit(solution)/shard_map/ppermute | solution.py:237
  12.0 0.9 copy-done.12
  12.9 0.8 collective-permute-start.3
  13.8 1.5 %collective-permute-start.2 = (bf16[2,9,32,128]{3,2,1,0:T(8,128)(2,1)S(1)}, bf16[2,9,32,128]{3,2,1,0:T(8,128)(2,1)}, u32[]{:S(2)}, u32[]{:S(2)}) collective-permute-start(bf16[2,9,32,128]{3,2,1,0:T(8,128)(2,1)S(1)} %shard_map.96.refs_0_), channel_id=1, source_target_pairs={{0,4},{1,9},{2,6},{3,11},{4,0},{5,13},{6,2},{7,15},{8,12},{9,1},{1... | collective-permute-start | bytes 442376 | tf_op jit(solution)/shard_map/ppermute | solution.py:241
  15.3 1.5 %collective-permute-start.1 = (bf16[2,9,32,128]{3,2,1,0:T(8,128)(2,1)S(1)}, bf16[2,9,32,128]{3,2,1,0:T(8,128)(2,1)}, u32[]{:S(2)}, u32[]{:S(2)}) collective-permute-start(bf16[2,9,32,128]{3,2,1,0:T(8,128)(2,1)S(1)} %shard_map.96.refs_0_), channel_id=1, source_target_pairs={{0,2},{1,5},{2,0},{3,7},{4,6},{5,1},{6,4},{7,3},{8,10},{9,13},{10,... | collective-permute-start | bytes 442376 | tf_op jit(solution)/shard_map/ppermute | solution.py:241
  16.8 4.8 %copy.10._.coupling_ref = bf16[128,96,96]{2,1,0:T(8,128)(2,1)} copy(bf16[128,96,96]{0,2,1:T(8,128)(2,1)} %param.12) | data formatting | bytes 4718592 | tf_op args[4]
  21.6 1.9 %copy-done.1 = bf16[128,96,96]{2,1,0:T(8,128)(2,1)S(1)} copy-done((bf16[128,96,96]{2,1,0:T(8,128)(2,1)S(1)}, bf16[128,96,96]{2,1,0:T(8,128)(2,1)}, u32[]{:S(2)}) %copy-start.1) | copy-done | bytes 2359320
  23.5 0.9 copy-done.8
  25.0 1.2 collective-permute-start.7
  26.1 1.8 %collective-permute-start.4 = (bf16[2,9,32,128]{3,2,1,0:T(8,128)(2,1)}, bf16[2,9,32,128]{3,2,1,0:T(8,128)(2,1)}, u32[]{:S(2)}, u32[]{:S(2)}) collective-permute-start(bf16[2,9,32,128]{3,2,1,0:T(8,128)(2,1)} %collective-permute-done.1.refs_1_), channel_id=1, source_target_pairs={{0,4},{1,9},{2,6},{3,11},{4,0},{5,13},{6,2},{7,15},{8,12},{9,1},{1... | collective-permute-start | bytes 442376 | tf_op jit(solution)/shard_map/ppermute | solution.py:241
  28.5 1.5 %collective-permute-start.5 = (bf16[2,9,32,128]{3,2,1,0:T(8,128)(2,1)}, bf16[2,9,32,128]{3,2,1,0:T(8,128)(2,1)}, u32[]{:S(2)}, u32[]{:S(2)}) collective-permute-start(bf16[2,9,32,128]{3,2,1,0:T(8,128)(2,1)} %collective-permute-done.3.refs_4_), channel_id=1, source_target_pairs={{0,2},{1,5},{2,0},{3,7},{4,6},{5,1},{6,4},{7,3},{8,10},{9,13},{10,... | collective-permute-start | bytes 442376 | tf_op jit(solution)/shard_map/ppermute | solution.py:241
  30.0 3.2 %collective-permute-done.7.refs_7_ = bf16[2,9,32,128]{3,2,1,0:T(8,128)(2,1)S(1)} collective-permute-done((bf16[2,9,32,128]{3,2,1,0:T(8,128)(2,1)S(1)}, bf16[2,9,32,128]{3,2,1,0:T(8,128)(2,1)S(1)}, u32[]{:S(2)}, u32[]{:S(2)}) %collective-permute-start.7) | collective-permute-done | bytes 147488 | tf_op jit(solution)/shard_map/ppermute | solution.py:241
  33.8 0.9 collective-permute-done.4.refs_3_
  38.2 1.9 %copy-done.2 = bf16[128,96,96]{2,1,0:T(8,128)(2,1)S(1)} copy-done((bf16[128,96,96]{2,1,0:T(8,128)(2,1)S(1)}, bf16[128,96,96]{2,1,0:T(8,128)(2,1)}, u32[]{:S(2)}) %copy-start.2) | copy-done | bytes 2359320
  40.1 0.9 copy-done.10
  41.0 5.3 %shard_map.98 = (bf16[4,2,9,32,128]{4,3,2,1,0:T(8,128)(2,1)S(1)}, bf16[4,2,9,32,128]{4,3,2,1,0:T(8,128)(2,1)S(1)}, bf16[4,2,9,32,128]{4,3,2,1,0:T(8,128)(2,1)S(1)}, bf16[4,2,9,32,128]{4,3,2,1,0:T(8,128)(2,1)}) custom-call(s32[128]{0:T(128)S(1)} %get-tuple-element.236.source_ref, s32[128]{0:T(128)S(1)} %get-tuple-element.237.target_ref, ...), custom_call_target="tpu_custom_call" | custom-call | flops 75497472 | bytes 10485760 | tf_op jit(solution)/shard_map/pallas_call | solution.py:373
  46.3 0.8 copy-done.6
  47.9 3.8 %collective-permute-start.17 = (bf16[1,32,256]{2,1,0:T(8,128)(2,1)S(1)}, bf16[1,32,256]{2,1,0:T(8,128)(2,1)S(1)}, u32[]{:S(2)}, u32[]{:S(2)}) collective-permute-start(bf16[1,32,256]{2,1,0:T(8,128)(2,1)S(1)} %copy-done.23), channel_id=1, source_target_pairs={{0,2},{1,3},{2,0},{3,1},{4,6},{5,7},{6,4},{7,5},{8,10},{9,11},{10,... | collective-permute-start | bytes 49160 | tf_op jit(solution)/shard_map/ppermute | solution.py:360
  54.4 1.6 %collective-permute-start.19 = (bf16[2,9,32,128]{3,2,1,0:T(8,128)(2,1)}, bf16[2,9,32,128]{3,2,1,0:T(8,128)(2,1)S(1)}, u32[]{:S(2)}, u32[]{:S(2)}) collective-permute-start(bf16[2,9,32,128]{3,2,1,0:T(8,128)(2,1)} %get-tuple-element.147), channel_id=1, source_target_pairs={{0,4},{1,9},{2,6},{3,11},{4,0},{5,13},{6,2},{7,15},{8,12},{9,1},{1... | collective-permute-start | bytes 442376 | tf_op jit(solution)/shard_map/ppermute | solution.py:241
  56.0 2.6 %collective-permute-start.20 = (bf16[2,9,32,128]{3,2,1,0:T(8,128)(2,1)}, bf16[2,9,32,128]{3,2,1,0:T(8,128)(2,1)}, u32[]{:S(2)}, u32[]{:S(2)}) collective-permute-start(bf16[2,9,32,128]{3,2,1,0:T(8,128)(2,1)} %get-tuple-element.148), channel_id=1, source_target_pairs={{0,8},{1,3},{2,10},{3,1},{4,12},{5,7},{6,14},{7,5},{8,0},{9,11},{1... | collective-permute-start | bytes 442376 | tf_op jit(solution)/shard_map/ppermute | solution.py:241
  58.6 1.7 %collective-permute-start.21 = (bf16[2,9,32,128]{3,2,1,0:T(8,128)(2,1)}, bf16[2,9,32,128]{3,2,1,0:T(8,128)(2,1)}, u32[]{:S(2)}, u32[]{:S(2)}) collective-permute-start(bf16[2,9,32,128]{3,2,1,0:T(8,128)(2,1)} %get-tuple-element.149), channel_id=1, source_target_pairs={{0,2},{1,5},{2,0},{3,7},{4,6},{5,1},{6,4},{7,3},{8,10},{9,13},{10,... | collective-permute-start | bytes 442376 | tf_op jit(solution)/shard_map/ppermute | solution.py:241
  61.7 0.9 collective-permute-done.20.refs_1_
  62.6 4.6 %collective-permute-done.21.refs_2_ = bf16[2,9,32,128]{3,2,1,0:T(8,128)(2,1)} collective-permute-done((bf16[2,9,32,128]{3,2,1,0:T(8,128)(2,1)}, bf16[2,9,32,128]{3,2,1,0:T(8,128)(2,1)}, u32[]{:S(2)}, u32[]{:S(2)}) %collective-permute-start.21) | collective-permute-done | bytes 147488 | tf_op jit(solution)/shard_map/ppermute | solution.py:241
  67.2 1.1 copy-done.7
  68.3 1.4 shard_map.100
  69.7 1.4 collective-permute-start.23
  71.1 1.1 collective-permute-start.24
  72.6 1.4 collective-permute-done.27.inner_ref
  74.1 1.0 collective-permute-done.28.outer_ref
  75.4 0.9 collective-permute-done.24.refs_1_
  76.3 1.1 collective-permute-done.25.refs_2_
  78.2 5.1 %collective-permute-done.29.rest_0_ = bf16[9,32,128]{2,1,0:T(8,128)(2,1)S(1)} collective-permute-done((bf16[9,32,128]{2,1,0:T(8,128)(2,1)S(1)}, bf16[9,32,128]{2,1,0:T(8,128)(2,1)S(1)}, u32[]{:S(2)}, u32[]{:S(2)}) %collective-permute-start.29) | collective-permute-done | bytes 73760 | tf_op jit(solution)/shard_map/ppermute | solution.py:237
  83.4 2.5 %shard_map.104 = (bf16[8,32,256]{2,1,0:T(8,128)(2,1)}, bf16[9,32,128]{2,1,0:T(8,128)(2,1)S(1)}, bf16[1,32,256]{2,1,0:T(8,128)(2,1)S(1)}, bf16[1,32,256]{2,1,0:T(8,128)(2,1)S(1)}) custom-call(s32[12]{0:T(128)S(1)} %copy-done.21, s32[1]{0:T(128)} %bitcast.core_ref, f32[8,32,256]{2,1,0:T(8,128)S(1)} %shard_map.97.near_ref, ...), custom_call_target="tpu_custom_call" | custom-call | tf_op jit(solution)/shard_map/pallas_call | solution.py:393
  86.1 5.2 %collective-permute-done.30.refs_1_ = bf16[9,32,128]{2,1,0:T(8,128)(2,1)S(1)} collective-permute-done((bf16[9,32,128]{2,1,0:T(8,128)(2,1)S(1)}, bf16[9,32,128]{2,1,0:T(8,128)(2,1)S(1)}, u32[]{:S(2)}, u32[]{:S(2)}) %collective-permute-start.30) | collective-permute-done | bytes 73760 | tf_op jit(solution)/shard_map/ppermute | solution.py:237
  91.4 1.0 collective-permute-start.32
  92.3 1.3 collective-permute-start.31
  93.6 0.9 copy-done.11
  95.1 2.7 %collective-permute-start.37 = (bf16[2,9,32,128]{3,2,1,0:T(8,128)(2,1)S(1)}, bf16[2,9,32,128]{3,2,1,0:T(8,128)(2,1)S(1)}, u32[]{:S(2)}, u32[]{:S(2)}) collective-permute-start(bf16[2,9,32,128]{3,2,1,0:T(8,128)(2,1)S(1)} %shard_map.105.refs_0_), channel_id=1, source_target_pairs={{0,14},{1,15},{2,12},{3,13},{4,10},{5,11},{6,8},{7,9},{8,6},{9,7},... | collective-permute-start | bytes 442376 | tf_op jit(solution)/shard_map/ppermute | solution.py:241
  98.0 1.1 collective-permute-done.32.refs_2_
  99.5 1.3 collective-permute-start.34
  100.8 0.9 collective-permute-start.36
  101.7 1.0 collective-permute-start.35
  103.2 1.4 collective-permute-done.34.refs_3_
  104.7 1.3 collective-permute-done.36.refs_6_
  106.0 0.9 collective-permute-done.35.refs_5_
  109.0 3.6 %shard_map.107 = (bf16[4,2,9,32,128]{4,3,2,1,0:T(8,128)(2,1)S(1)}, bf16[4,2,9,32,128]{4,3,2,1,0:T(8,128)(2,1)S(1)}, bf16[4,2,9,32,128]{4,3,2,1,0:T(8,128)(2,1)S(1)}, bf16[4,2,9,32,128]{4,3,2,1,0:T(8,128)(2,1)S(1)}) custom-call(s32[128]{0:T(128)S(1)} %copy-done.18, s32[128]{0:T(128)S(1)} %copy-done.20, bf16[128,96,96]{2,1,0:T(8,128)(2,1)S(1)} %copy-done.3, ...), custom_call_target="tpu_custom_call" | custom-call | flops 75497472 | bytes 10485760 | tf_op jit(solution)/shard_map/pallas_call | solution.py:373
  113.6 3.7 %collective-permute-start.47 = (bf16[1,32,256]{2,1,0:T(8,128)(2,1)S(1)}, bf16[1,32,256]{2,1,0:T(8,128)(2,1)S(1)}, u32[]{:S(2)}, u32[]{:S(2)}) collective-permute-start(bf16[1,32,256]{2,1,0:T(8,128)(2,1)S(1)} %get-tuple-element.205), channel_id=1, source_target_pairs={{0,2},{1,3},{2,0},{3,1},{4,6},{5,7},{6,4},{7,5},{8,10},{9,11},{10,... | collective-permute-start | bytes 49160 | tf_op jit(solution)/shard_map/ppermute | solution.py:360
  117.5 1.6 %collective-permute-done.47.first_ref = bf16[1,32,256]{2,1,0:T(8,128)(2,1)S(1)} collective-permute-done((bf16[1,32,256]{2,1,0:T(8,128)(2,1)S(1)}, bf16[1,32,256]{2,1,0:T(8,128)(2,1)S(1)}, u32[]{:S(2)}, u32[]{:S(2)}) %collective-permute-start.47) | collective-permute-done | bytes 16416 | tf_op jit(solution)/shard_map/ppermute | solution.py:360
  119.1 2.0 %collective-permute-start.49 = (bf16[2,9,32,128]{3,2,1,0:T(8,128)(2,1)S(1)}, bf16[2,9,32,128]{3,2,1,0:T(8,128)(2,1)S(1)}, u32[]{:S(2)}, u32[]{:S(2)}) collective-permute-start(bf16[2,9,32,128]{3,2,1,0:T(8,128)(2,1)S(1)} %get-tuple-element.206), channel_id=1, source_target_pairs={{0,4},{1,9},{2,6},{3,11},{4,0},{5,13},{6,2},{7,15},{8,12},{9,1},{1... | collective-permute-start | bytes 442376 | tf_op jit(solution)/shard_map/ppermute | solution.py:241
  121.1 1.9 %collective-permute-start.50 = (bf16[2,9,32,128]{3,2,1,0:T(8,128)(2,1)S(1)}, bf16[2,9,32,128]{3,2,1,0:T(8,128)(2,1)S(1)}, u32[]{:S(2)}, u32[]{:S(2)}) collective-permute-start(bf16[2,9,32,128]{3,2,1,0:T(8,128)(2,1)S(1)} %get-tuple-element.207), channel_id=1, source_target_pairs={{0,8},{1,3},{2,10},{3,1},{4,12},{5,7},{6,14},{7,5},{8,0},{9,11},{1... | collective-permute-start | bytes 442376 | tf_op jit(solution)/shard_map/ppermute | solution.py:241
  123.1 2.0 %collective-permute-start.51 = (bf16[2,9,32,128]{3,2,1,0:T(8,128)(2,1)S(1)}, bf16[2,9,32,128]{3,2,1,0:T(8,128)(2,1)S(1)}, u32[]{:S(2)}, u32[]{:S(2)}) collective-permute-start(bf16[2,9,32,128]{3,2,1,0:T(8,128)(2,1)S(1)} %get-tuple-element.208), channel_id=1, source_target_pairs={{0,2},{1,5},{2,0},{3,7},{4,6},{5,1},{6,4},{7,3},{8,10},{9,13},{10,... | collective-permute-start | bytes 442376 | tf_op jit(solution)/shard_map/ppermute | solution.py:241
  125.1 1.2 collective-permute-done.50.refs_1_
  126.3 5.1 %collective-permute-done.51.refs_2_ = bf16[2,9,32,128]{3,2,1,0:T(8,128)(2,1)S(1)} collective-permute-done((bf16[2,9,32,128]{3,2,1,0:T(8,128)(2,1)S(1)}, bf16[2,9,32,128]{3,2,1,0:T(8,128)(2,1)S(1)}, u32[]{:S(2)}, u32[]{:S(2)}) %collective-permute-start.51) | collective-permute-done | bytes 147488 | tf_op jit(solution)/shard_map/ppermute | solution.py:241
  131.6 1.8 %collective-permute-start.53 = (bf16[2,9,32,128]{3,2,1,0:T(8,128)(2,1)S(1)}, bf16[2,9,32,128]{3,2,1,0:T(8,128)(2,1)S(1)}, u32[]{:S(2)}, u32[]{:S(2)}) collective-permute-start(bf16[2,9,32,128]{3,2,1,0:T(8,128)(2,1)S(1)} %get-tuple-element.222), channel_id=1, source_target_pairs={{0,2},{1,5},{2,0},{3,7},{4,6},{5,1},{6,4},{7,3},{8,10},{9,13},{10,... | collective-permute-start | bytes 442376 | tf_op jit(solution)/shard_map/ppermute | solution.py:241
  133.3 1.2 collective-permute-start.54
  134.8 1.2 collective-permute-done.57.inner_ref
  136.1 1.0 collective-permute-done.58.outer_ref
  137.6 0.8 collective-permute-done.54.refs_1_
  138.5 1.2 collective-permute-done.55.refs_2_
  139.7 1.8 %collective-permute-start.59 = (bf16[9,32,128]{2,1,0:T(8,128)(2,1)S(1)}, bf16[9,32,128]{2,1,0:T(8,128)(2,1)S(1)}, u32[]{:S(2)}, u32[]{:S(2)}) collective-permute-start(bf16[9,32,128]{2,1,0:T(8,128)(2,1)S(1)} %get-tuple-element.235), channel_id=1, source_target_pairs={{0,16},{1,17},{2,18},{3,19},{4,20},{5,21},{6,22},{7,23},{8,24},{9,... | collective-permute-start | bytes 221192 | tf_op jit(solution)/shard_map/ppermute | solution.py:237
  141.5 4.1 %collective-permute-done.59.rest_0_ = bf16[9,32,128]{2,1,0:T(8,128)(2,1)S(1)} collective-permute-done((bf16[9,32,128]{2,1,0:T(8,128)(2,1)S(1)}, bf16[9,32,128]{2,1,0:T(8,128)(2,1)S(1)}, u32[]{:S(2)}, u32[]{:S(2)}) %collective-permute-start.59) | collective-permute-done | bytes 73760 | tf_op jit(solution)/shard_map/ppermute | solution.py:237
  145.7 2.5 %shard_map.113 = bf16[8,32,256]{2,1,0:T(8,128)(2,1)} custom-call(s32[12]{0:T(128)S(1)} %copy-done.21, s32[1]{0:T(128)} %bitcast.core_ref, f32[8,32,256]{2,1,0:T(8,128)S(1)} %shard_map.106.near_ref, f32[2,32,256]{2,1,0:T(8,128)S(1)} %shard_map.111.edge_ref, bf16[8,96,256]{2,1,0:T(8,128)(2,1)S(1)} %copy-done.4, bf16[8,96,96]{2,1,0:T(8,128)(2,1)S(1)} %copy-done.5, ...), custom_call_target="tpu_custom_call" | custom-call | tf_op jit(solution)/shard_map/pallas_call | solution.py:393
  (125 shorter events, 18.2 us)
Async XLA Ops:
  0.6 20.9 %copy-start = (bf16[8,3,256,256]{3,2,1,0:T(8,128)(2,1)S(1)}, bf16[8,3,256,256]{3,2,1,0:T(8,128)(2,1)}, u32[]{:S(2)}) copy-start(bf16[8,3,256,256]{3,2,1,0:T(8,128)(2,1)} %last_ref.3) | copy-start | bytes 9437188
  3.8 8.2 %collective-permute-start = (bf16[9,32,128]{2,1,0:T(8,128)(2,1)}, bf16[9,32,128]{2,1,0:T(8,128)(2,1)S(1)}, u32[]{:S(2)}, u32[]{:S(2)}) collective-permute-start(bf16[9,32,128]{2,1,0:T(8,128)(2,1)} %get-tuple-element.119.refs_0_), channel_id=1, source_target_pairs={{0,16},{1,17},{2,18},{3,19},{4,20},{5,21},{6,22},{7,23},{8,24},{9,... | collective-permute-start | bytes 221192 | tf_op jit(solution)/shard_map/ppermute | solution.py:237
  12.9 13.2 %collective-permute-start.3 = (bf16[2,9,32,128]{3,2,1,0:T(8,128)(2,1)S(1)}, bf16[2,9,32,128]{3,2,1,0:T(8,128)(2,1)}, u32[]{:S(2)}, u32[]{:S(2)}) collective-permute-start(bf16[2,9,32,128]{3,2,1,0:T(8,128)(2,1)S(1)} %shard_map.96.refs_0_), channel_id=1, source_target_pairs={{0,8},{1,3},{2,10},{3,1},{4,12},{5,7},{6,14},{7,5},{8,0},{9,11},{1... | collective-permute-start | bytes 442376 | tf_op jit(solution)/shard_map/ppermute | solution.py:241
  13.8 12.4 %collective-permute-start.2 = (bf16[2,9,32,128]{3,2,1,0:T(8,128)(2,1)S(1)}, bf16[2,9,32,128]{3,2,1,0:T(8,128)(2,1)}, u32[]{:S(2)}, u32[]{:S(2)}) collective-permute-start(bf16[2,9,32,128]{3,2,1,0:T(8,128)(2,1)S(1)} %shard_map.96.refs_0_), channel_id=1, source_target_pairs={{0,4},{1,9},{2,6},{3,11},{4,0},{5,13},{6,2},{7,15},{8,12},{9,1},{1... | collective-permute-start | bytes 442376 | tf_op jit(solution)/shard_map/ppermute | solution.py:241
  15.3 10.9 %collective-permute-start.1 = (bf16[2,9,32,128]{3,2,1,0:T(8,128)(2,1)S(1)}, bf16[2,9,32,128]{3,2,1,0:T(8,128)(2,1)}, u32[]{:S(2)}, u32[]{:S(2)}) collective-permute-start(bf16[2,9,32,128]{3,2,1,0:T(8,128)(2,1)S(1)} %shard_map.96.refs_0_), channel_id=1, source_target_pairs={{0,2},{1,5},{2,0},{3,7},{4,6},{5,1},{6,4},{7,3},{8,10},{9,13},{10,... | collective-permute-start | bytes 442376 | tf_op jit(solution)/shard_map/ppermute | solution.py:241
  25.0 8.2 %collective-permute-start.7 = (bf16[2,9,32,128]{3,2,1,0:T(8,128)(2,1)S(1)}, bf16[2,9,32,128]{3,2,1,0:T(8,128)(2,1)S(1)}, u32[]{:S(2)}, u32[]{:S(2)}) collective-permute-start(bf16[2,9,32,128]{3,2,1,0:T(8,128)(2,1)S(1)} %shard_map.96.refs_0_), channel_id=1, source_target_pairs={{0,14},{1,15},{2,12},{3,13},{4,10},{5,11},{6,8},{7,9},{8,6},{9,7},... | collective-permute-start | bytes 442376 | tf_op jit(solution)/shard_map/ppermute | solution.py:241
  26.1 8.6 %collective-permute-start.4 = (bf16[2,9,32,128]{3,2,1,0:T(8,128)(2,1)}, bf16[2,9,32,128]{3,2,1,0:T(8,128)(2,1)}, u32[]{:S(2)}, u32[]{:S(2)}) collective-permute-start(bf16[2,9,32,128]{3,2,1,0:T(8,128)(2,1)} %collective-permute-done.1.refs_1_), channel_id=1, source_target_pairs={{0,4},{1,9},{2,6},{3,11},{4,0},{5,13},{6,2},{7,15},{8,12},{9,1},{1... | collective-permute-start | bytes 442376 | tf_op jit(solution)/shard_map/ppermute | solution.py:241
  27.9 6.8 %collective-permute-start.6 = (bf16[2,9,32,128]{3,2,1,0:T(8,128)(2,1)}, bf16[2,9,32,128]{3,2,1,0:T(8,128)(2,1)}, u32[]{:S(2)}, u32[]{:S(2)}) collective-permute-start(bf16[2,9,32,128]{3,2,1,0:T(8,128)(2,1)} %collective-permute-done.2.refs_2_), channel_id=1, source_target_pairs={{0,8},{1,3},{2,10},{3,1},{4,12},{5,7},{6,14},{7,5},{8,0},{9,11},{1... | collective-permute-start | bytes 442376 | tf_op jit(solution)/shard_map/ppermute | solution.py:241
  28.5 6.8 %collective-permute-start.5 = (bf16[2,9,32,128]{3,2,1,0:T(8,128)(2,1)}, bf16[2,9,32,128]{3,2,1,0:T(8,128)(2,1)}, u32[]{:S(2)}, u32[]{:S(2)}) collective-permute-start(bf16[2,9,32,128]{3,2,1,0:T(8,128)(2,1)} %collective-permute-done.3.refs_4_), channel_id=1, source_target_pairs={{0,2},{1,5},{2,0},{3,7},{4,6},{5,1},{6,4},{7,3},{8,10},{9,13},{10,... | collective-permute-start | bytes 442376 | tf_op jit(solution)/shard_map/ppermute | solution.py:241
  30.0 5.3 %collective-permute-start.8 = (bf16[2,9,32,128]{3,2,1,0:T(8,128)(2,1)S(1)}, bf16[2,9,32,128]{3,2,1,0:T(8,128)(2,1)}, u32[]{:S(2)}, u32[]{:S(2)}) collective-permute-start(bf16[2,9,32,128]{3,2,1,0:T(8,128)(2,1)S(1)} %shard_map.96.refs_0_), channel_id=1, source_target_pairs={{0,1},{1,0},{2,3},{3,2},{4,5},{5,4},{6,7},{7,6},{8,9},{9,8},{10,11... | collective-permute-start | bytes 442376 | tf_op jit(solution)/shard_map/ppermute | solution.py:246
  33.8 1.9 %collective-permute-start.9 = (bf16[2,9,32,128]{3,2,1,0:T(8,128)(2,1)}, bf16[2,9,32,128]{3,2,1,0:T(8,128)(2,1)}, u32[]{:S(2)}, u32[]{:S(2)}) collective-permute-start(bf16[2,9,32,128]{3,2,1,0:T(8,128)(2,1)} %collective-permute-done.1.refs_1_), channel_id=1, source_target_pairs={{0,1},{1,0},{2,3},{3,2},{4,5},{5,4},{6,7},{7,6},{8,9},{9,8},{10,11... | collective-permute-start | bytes 442376 | tf_op jit(solution)/shard_map/ppermute | solution.py:246
  34.7 1.8 %collective-permute-start.10 = (bf16[2,9,32,128]{3,2,1,0:T(8,128)(2,1)}, bf16[2,9,32,128]{3,2,1,0:T(8,128)(2,1)}, u32[]{:S(2)}, u32[]{:S(2)}) collective-permute-start(bf16[2,9,32,128]{3,2,1,0:T(8,128)(2,1)} %collective-permute-done.2.refs_2_), channel_id=1, source_target_pairs={{0,1},{1,0},{2,3},{3,2},{4,5},{5,4},{6,7},{7,6},{8,9},{9,8},{10,11... | collective-permute-start | bytes 442376 | tf_op jit(solution)/shard_map/ppermute | solution.py:246
  34.7 2.7 %collective-permute-start.12 = (bf16[2,9,32,128]{3,2,1,0:T(8,128)(2,1)}, bf16[2,9,32,128]{3,2,1,0:T(8,128)(2,1)S(1)}, u32[]{:S(2)}, u32[]{:S(2)}) collective-permute-start(bf16[2,9,32,128]{3,2,1,0:T(8,128)(2,1)} %collective-permute-done.3.refs_4_), channel_id=1, source_target_pairs={{0,1},{1,0},{2,3},{3,2},{4,5},{5,4},{6,7},{7,6},{8,9},{9,8},{10,11... | collective-permute-start | bytes 442376 | tf_op jit(solution)/shard_map/ppermute | solution.py:246
  35.2 2.2 %collective-permute-start.11 = (bf16[2,9,32,128]{3,2,1,0:T(8,128)(2,1)}, bf16[2,9,32,128]{3,2,1,0:T(8,128)(2,1)S(1)}, u32[]{:S(2)}, u32[]{:S(2)}) collective-permute-start(bf16[2,9,32,128]{3,2,1,0:T(8,128)(2,1)} %collective-permute-done.4.refs_3_), channel_id=1, source_target_pairs={{0,1},{1,0},{2,3},{3,2},{4,5},{5,4},{6,7},{7,6},{8,9},{9,8},{10,11... | collective-permute-start | bytes 442376 | tf_op jit(solution)/shard_map/ppermute | solution.py:246
  35.3 2.2 %collective-permute-start.13 = (bf16[2,9,32,128]{3,2,1,0:T(8,128)(2,1)}, bf16[2,9,32,128]{3,2,1,0:T(8,128)(2,1)S(1)}, u32[]{:S(2)}, u32[]{:S(2)}) collective-permute-start(bf16[2,9,32,128]{3,2,1,0:T(8,128)(2,1)} %collective-permute-done.5.refs_5_), channel_id=1, source_target_pairs={{0,1},{1,0},{2,3},{3,2},{4,5},{5,4},{6,7},{7,6},{8,9},{9,8},{10,11... | collective-permute-start | bytes 442376 | tf_op jit(solution)/shard_map/ppermute | solution.py:246
  35.8 1.7 %collective-permute-start.14 = (bf16[2,9,32,128]{3,2,1,0:T(8,128)(2,1)}, bf16[2,9,32,128]{3,2,1,0:T(8,128)(2,1)S(1)}, u32[]{:S(2)}, u32[]{:S(2)}) collective-permute-start(bf16[2,9,32,128]{3,2,1,0:T(8,128)(2,1)} %collective-permute-done.6.refs_6_), channel_id=1, source_target_pairs={{0,1},{1,0},{2,3},{3,2},{4,5},{5,4},{6,7},{7,6},{8,9},{9,8},{10,11... | collective-permute-start | bytes 442376 | tf_op jit(solution)/shard_map/ppermute | solution.py:246
  36.6 1.6 %collective-permute-start.15 = (bf16[2,9,32,128]{3,2,1,0:T(8,128)(2,1)}, bf16[2,9,32,128]{3,2,1,0:T(8,128)(2,1)S(1)}, u32[]{:S(2)}, u32[]{:S(2)}) collective-permute-start(bf16[2,9,32,128]{3,2,1,0:T(8,128)(2,1)} %copy-done.9), channel_id=1, source_target_pairs={{0,1},{1,0},{2,3},{3,2},{4,5},{5,4},{6,7},{7,6},{8,9},{9,8},{10,11... | collective-permute-start | bytes 442376 | tf_op jit(solution)/shard_map/ppermute | solution.py:246
  37.4 15.1 %copy-start.17 = (s32[128]{0:T(128)}, s32[128]{0:T(128)S(1)}, u32[]{:S(2)}) copy-start(s32[128]{0:T(128)S(1)} %get-tuple-element.236.source_ref) | copy-start | bytes 1540
  37.4 15.1 %copy-start.19 = (s32[128]{0:T(128)}, s32[128]{0:T(128)S(1)}, u32[]{:S(2)}) copy-start(s32[128]{0:T(128)S(1)} %get-tuple-element.237.target_ref) | copy-start | bytes 1540
  47.1 4.6 %collective-permute-start.16 = (bf16[4,2,9,32,128]{4,3,2,1,0:T(8,128)(2,1)S(1)}, bf16[4,2,9,32,128]{4,3,2,1,0:T(8,128)(2,1)S(1)}, u32[]{:S(2)}, u32[]{:S(2)}) collective-permute-start(bf16[4,2,9,32,128]{4,3,2,1,0:T(8,128)(2,1)S(1)} %get-tuple-element.140), channel_id=1, source_target_pairs={{0,1},{1,0},{2,3},{3,2},{4,5},{5,4},{6,7},{7,6},{8,9},{9,8},{10,11... | collective-permute-start | bytes 1769480 | tf_op jit(solution)/shard_map/ppermute | solution.py:246
  47.2 5.9 %collective-permute-start.18 = (bf16[1,32,256]{2,1,0:T(8,128)(2,1)S(1)}, bf16[1,32,256]{2,1,0:T(8,128)(2,1)S(1)}, u32[]{:S(2)}, u32[]{:S(2)}) collective-permute-start(bf16[1,32,256]{2,1,0:T(8,128)(2,1)S(1)} %copy-done.23), channel_id=1, source_target_pairs={{2,4},{3,5},{4,2},{5,3},{6,8},{7,9},{8,6},{9,7},{10,12},{11,13},{1... | collective-permute-start | bytes 49160 | tf_op jit(solution)/shard_map/ppermute | solution.py:360
  47.9 5.9 %collective-permute-start.17 = (bf16[1,32,256]{2,1,0:T(8,128)(2,1)S(1)}, bf16[1,32,256]{2,1,0:T(8,128)(2,1)S(1)}, u32[]{:S(2)}, u32[]{:S(2)}) collective-permute-start(bf16[1,32,256]{2,1,0:T(8,128)(2,1)S(1)} %copy-done.23), channel_id=1, source_target_pairs={{0,2},{1,3},{2,0},{3,1},{4,6},{5,7},{6,4},{7,5},{8,10},{9,11},{10,... | collective-permute-start | bytes 49160 | tf_op jit(solution)/shard_map/ppermute | solution.py:360
  54.4 12.8 %collective-permute-start.22 = (bf16[4,2,9,32,128]{4,3,2,1,0:T(8,128)(2,1)}, bf16[4,2,9,32,128]{4,3,2,1,0:T(8,128)(2,1)}, u32[]{:S(2)}, u32[]{:S(2)}) collective-permute-start(bf16[4,2,9,32,128]{4,3,2,1,0:T(8,128)(2,1)} %get-tuple-element.150), channel_id=1, source_target_pairs={{0,1},{1,0},{2,3},{3,2},{4,5},{5,4},{6,7},{7,6},{8,9},{9,8},{10,11... | collective-permute-start | bytes 1769480 | tf_op jit(solution)/shard_map/ppermute | solution.py:246
  54.4 7.3 %collective-permute-start.19 = (bf16[2,9,32,128]{3,2,1,0:T(8,128)(2,1)}, bf16[2,9,32,128]{3,2,1,0:T(8,128)(2,1)S(1)}, u32[]{:S(2)}, u32[]{:S(2)}) collective-permute-start(bf16[2,9,32,128]{3,2,1,0:T(8,128)(2,1)} %get-tuple-element.147), channel_id=1, source_target_pairs={{0,4},{1,9},{2,6},{3,11},{4,0},{5,13},{6,2},{7,15},{8,12},{9,1},{1... | collective-permute-start | bytes 442376 | tf_op jit(solution)/shard_map/ppermute | solution.py:241
  56.0 6.6 %collective-permute-start.20 = (bf16[2,9,32,128]{3,2,1,0:T(8,128)(2,1)}, bf16[2,9,32,128]{3,2,1,0:T(8,128)(2,1)}, u32[]{:S(2)}, u32[]{:S(2)}) collective-permute-start(bf16[2,9,32,128]{3,2,1,0:T(8,128)(2,1)} %get-tuple-element.148), channel_id=1, source_target_pairs={{0,8},{1,3},{2,10},{3,1},{4,12},{5,7},{6,14},{7,5},{8,0},{9,11},{1... | collective-permute-start | bytes 442376 | tf_op jit(solution)/shard_map/ppermute | solution.py:241
  58.6 8.6 %collective-permute-start.21 = (bf16[2,9,32,128]{3,2,1,0:T(8,128)(2,1)}, bf16[2,9,32,128]{3,2,1,0:T(8,128)(2,1)}, u32[]{:S(2)}, u32[]{:S(2)}) collective-permute-start(bf16[2,9,32,128]{3,2,1,0:T(8,128)(2,1)} %get-tuple-element.149), channel_id=1, source_target_pairs={{0,2},{1,5},{2,0},{3,7},{4,6},{5,1},{6,4},{7,3},{8,10},{9,13},{10,... | collective-permute-start | bytes 442376 | tf_op jit(solution)/shard_map/ppermute | solution.py:241
  60.3 15.0 %collective-permute-start.26 = (bf16[2,9,32,128]{3,2,1,0:T(8,128)(2,1)}, bf16[2,9,32,128]{3,2,1,0:T(8,128)(2,1)S(1)}, u32[]{:S(2)}, u32[]{:S(2)}) collective-permute-start(bf16[2,9,32,128]{3,2,1,0:T(8,128)(2,1)} %copy-done.22), channel_id=1, source_target_pairs={{0,14},{1,15},{2,12},{3,13},{4,10},{5,11},{6,8},{7,9},{8,6},{9,7},... | collective-permute-start | bytes 442376 | tf_op jit(solution)/shard_map/ppermute | solution.py:241
  69.7 24.0 %copy-start.3 = (bf16[128,96,96]{2,1,0:T(8,128)(2,1)S(1)}, bf16[128,96,96]{2,1,0:T(8,128)(2,1)}, u32[]{:S(2)}) copy-start(bf16[128,96,96]{2,1,0:T(8,128)(2,1)} %copy.10._.coupling_ref) | copy-start | bytes 7077892
  69.7 5.7 %collective-permute-start.23 = (bf16[2,9,32,128]{3,2,1,0:T(8,128)(2,1)S(1)}, bf16[2,9,32,128]{3,2,1,0:T(8,128)(2,1)S(1)}, u32[]{:S(2)}, u32[]{:S(2)}) collective-permute-start(bf16[2,9,32,128]{3,2,1,0:T(8,128)(2,1)S(1)} %get-tuple-element.163), channel_id=1, source_target_pairs={{0,2},{1,5},{2,0},{3,7},{4,6},{5,1},{6,4},{7,3},{8,10},{9,13},{10,... | collective-permute-start | bytes 442376 | tf_op jit(solution)/shard_map/ppermute | solution.py:241
  71.1 5.1 %collective-permute-start.24 = (bf16[2,9,32,128]{3,2,1,0:T(8,128)(2,1)S(1)}, bf16[2,9,32,128]{3,2,1,0:T(8,128)(2,1)S(1)}, u32[]{:S(2)}, u32[]{:S(2)}) collective-permute-start(bf16[2,9,32,128]{3,2,1,0:T(8,128)(2,1)S(1)} %get-tuple-element.164), channel_id=1, source_target_pairs={{0,4},{1,9},{2,6},{3,11},{4,0},{5,13},{6,2},{7,15},{8,12},{9,1},{1... | collective-permute-start | bytes 442376 | tf_op jit(solution)/shard_map/ppermute | solution.py:241
  72.3 5.1 %collective-permute-start.25 = (bf16[2,9,32,128]{3,2,1,0:T(8,128)(2,1)S(1)}, bf16[2,9,32,128]{3,2,1,0:T(8,128)(2,1)S(1)}, u32[]{:S(2)}, u32[]{:S(2)}) collective-permute-start(bf16[2,9,32,128]{3,2,1,0:T(8,128)(2,1)S(1)} %get-tuple-element.165), channel_id=1, source_target_pairs={{0,8},{1,3},{2,10},{3,1},{4,12},{5,7},{6,14},{7,5},{8,0},{9,11},{1... | collective-permute-start | bytes 442376 | tf_op jit(solution)/shard_map/ppermute | solution.py:241
  72.6 1.4 collective-permute-start.27
  74.0 1.2 collective-permute-start.28
  77.5 5.8 %collective-permute-start.29 = (bf16[9,32,128]{2,1,0:T(8,128)(2,1)S(1)}, bf16[9,32,128]{2,1,0:T(8,128)(2,1)S(1)}, u32[]{:S(2)}, u32[]{:S(2)}) collective-permute-start(bf16[9,32,128]{2,1,0:T(8,128)(2,1)S(1)} %get-tuple-element.176), channel_id=1, source_target_pairs={{0,16},{1,17},{2,18},{3,19},{4,20},{5,21},{6,22},{7,23},{8,24},{9,... | collective-permute-start | bytes 221192 | tf_op jit(solution)/shard_map/ppermute | solution.py:237
  85.9 5.4 %collective-permute-start.30 = (bf16[9,32,128]{2,1,0:T(8,128)(2,1)S(1)}, bf16[9,32,128]{2,1,0:T(8,128)(2,1)S(1)}, u32[]{:S(2)}, u32[]{:S(2)}) collective-permute-start(bf16[9,32,128]{2,1,0:T(8,128)(2,1)S(1)} %get-tuple-element.178.refs_0_), channel_id=1, source_target_pairs={{0,16},{1,17},{2,18},{3,19},{4,20},{5,21},{6,22},{7,23},{8,24},{9,... | collective-permute-start | bytes 221192 | tf_op jit(solution)/shard_map/ppermute | solution.py:237
  91.3 6.7 %collective-permute-start.33 = (bf16[2,9,32,128]{3,2,1,0:T(8,128)(2,1)S(1)}, bf16[2,9,32,128]{3,2,1,0:T(8,128)(2,1)S(1)}, u32[]{:S(2)}, u32[]{:S(2)}) collective-permute-start(bf16[2,9,32,128]{3,2,1,0:T(8,128)(2,1)S(1)} %shard_map.105.refs_0_), channel_id=1, source_target_pairs={{0,8},{1,3},{2,10},{3,1},{4,12},{5,7},{6,14},{7,5},{8,0},{9,11},{1... | collective-permute-start | bytes 442376 | tf_op jit(solution)/shard_map/ppermute | solution.py:241
  91.4 7.7 %collective-permute-start.32 = (bf16[2,9,32,128]{3,2,1,0:T(8,128)(2,1)S(1)}, bf16[2,9,32,128]{3,2,1,0:T(8,128)(2,1)S(1)}, u32[]{:S(2)}, u32[]{:S(2)}) collective-permute-start(bf16[2,9,32,128]{3,2,1,0:T(8,128)(2,1)S(1)} %shard_map.105.refs_0_), channel_id=1, source_target_pairs={{0,4},{1,9},{2,6},{3,11},{4,0},{5,13},{6,2},{7,15},{8,12},{9,1},{1... | collective-permute-start | bytes 442376 | tf_op jit(solution)/shard_map/ppermute | solution.py:241
  92.3 7.2 %collective-permute-start.31 = (bf16[2,9,32,128]{3,2,1,0:T(8,128)(2,1)S(1)}, bf16[2,9,32,128]{3,2,1,0:T(8,128)(2,1)S(1)}, u32[]{:S(2)}, u32[]{:S(2)}) collective-permute-start(bf16[2,9,32,128]{3,2,1,0:T(8,128)(2,1)S(1)} %shard_map.105.refs_0_), channel_id=1, source_target_pairs={{0,2},{1,5},{2,0},{3,7},{4,6},{5,1},{6,4},{7,3},{8,10},{9,13},{10,... | collective-permute-start | bytes 442376 | tf_op jit(solution)/shard_map/ppermute | solution.py:241
  95.1 7.6 %collective-permute-start.37 = (bf16[2,9,32,128]{3,2,1,0:T(8,128)(2,1)S(1)}, bf16[2,9,32,128]{3,2,1,0:T(8,128)(2,1)S(1)}, u32[]{:S(2)}, u32[]{:S(2)}) collective-permute-start(bf16[2,9,32,128]{3,2,1,0:T(8,128)(2,1)S(1)} %shard_map.105.refs_0_), channel_id=1, source_target_pairs={{0,14},{1,15},{2,12},{3,13},{4,10},{5,11},{6,8},{7,9},{8,6},{9,7},... | collective-permute-start | bytes 442376 | tf_op jit(solution)/shard_map/ppermute | solution.py:241
  99.5 5.1 %collective-permute-start.34 = (bf16[2,9,32,128]{3,2,1,0:T(8,128)(2,1)S(1)}, bf16[2,9,32,128]{3,2,1,0:T(8,128)(2,1)S(1)}, u32[]{:S(2)}, u32[]{:S(2)}) collective-permute-start(bf16[2,9,32,128]{3,2,1,0:T(8,128)(2,1)S(1)} %collective-permute-done.31.refs_1_), channel_id=1, source_target_pairs={{0,4},{1,9},{2,6},{3,11},{4,0},{5,13},{6,2},{7,15},{8,12},{9,1},{1... | collective-permute-start | bytes 442376 | tf_op jit(solution)/shard_map/ppermute | solution.py:241
  100.8 5.1 %collective-permute-start.36 = (bf16[2,9,32,128]{3,2,1,0:T(8,128)(2,1)S(1)}, bf16[2,9,32,128]{3,2,1,0:T(8,128)(2,1)S(1)}, u32[]{:S(2)}, u32[]{:S(2)}) collective-permute-start(bf16[2,9,32,128]{3,2,1,0:T(8,128)(2,1)S(1)} %collective-permute-done.32.refs_2_), channel_id=1, source_target_pairs={{0,8},{1,3},{2,10},{3,1},{4,12},{5,7},{6,14},{7,5},{8,0},{9,11},{1... | collective-permute-start | bytes 442376 | tf_op jit(solution)/shard_map/ppermute | solution.py:241
  101.7 5.1 %collective-permute-start.35 = (bf16[2,9,32,128]{3,2,1,0:T(8,128)(2,1)S(1)}, bf16[2,9,32,128]{3,2,1,0:T(8,128)(2,1)S(1)}, u32[]{:S(2)}, u32[]{:S(2)}) collective-permute-start(bf16[2,9,32,128]{3,2,1,0:T(8,128)(2,1)S(1)} %collective-permute-done.33.refs_4_), channel_id=1, source_target_pairs={{0,2},{1,5},{2,0},{3,7},{4,6},{5,1},{6,4},{7,3},{8,10},{9,13},{10,... | collective-permute-start | bytes 442376 | tf_op jit(solution)/shard_map/ppermute | solution.py:241
  102.7 4.2 %collective-permute-start.38 = (bf16[2,9,32,128]{3,2,1,0:T(8,128)(2,1)S(1)}, bf16[2,9,32,128]{3,2,1,0:T(8,128)(2,1)S(1)}, u32[]{:S(2)}, u32[]{:S(2)}) collective-permute-start(bf16[2,9,32,128]{3,2,1,0:T(8,128)(2,1)S(1)} %shard_map.105.refs_0_), channel_id=1, source_target_pairs={{0,1},{1,0},{2,3},{3,2},{4,5},{5,4},{6,7},{7,6},{8,9},{9,8},{10,11... | collective-permute-start | bytes 442376 | tf_op jit(solution)/shard_map/ppermute | solution.py:246
  102.7 4.7 %collective-permute-start.39 = (bf16[2,9,32,128]{3,2,1,0:T(8,128)(2,1)S(1)}, bf16[2,9,32,128]{3,2,1,0:T(8,128)(2,1)S(1)}, u32[]{:S(2)}, u32[]{:S(2)}) collective-permute-start(bf16[2,9,32,128]{3,2,1,0:T(8,128)(2,1)S(1)} %collective-permute-done.31.refs_1_), channel_id=1, source_target_pairs={{0,1},{1,0},{2,3},{3,2},{4,5},{5,4},{6,7},{7,6},{8,9},{9,8},{10,11... | collective-permute-start | bytes 442376 | tf_op jit(solution)/shard_map/ppermute | solution.py:246
  104.7 2.8 %collective-permute-start.40 = (bf16[2,9,32,128]{3,2,1,0:T(8,128)(2,1)S(1)}, bf16[2,9,32,128]{3,2,1,0:T(8,128)(2,1)S(1)}, u32[]{:S(2)}, u32[]{:S(2)}) collective-permute-start(bf16[2,9,32,128]{3,2,1,0:T(8,128)(2,1)S(1)} %collective-permute-done.32.refs_2_), channel_id=1, source_target_pairs={{0,1},{1,0},{2,3},{3,2},{4,5},{5,4},{6,7},{7,6},{8,9},{9,8},{10,11... | collective-permute-start | bytes 442376 | tf_op jit(solution)/shard_map/ppermute | solution.py:246
  106.0 2.0 %collective-permute-start.42 = (bf16[2,9,32,128]{3,2,1,0:T(8,128)(2,1)S(1)}, bf16[2,9,32,128]{3,2,1,0:T(8,128)(2,1)S(1)}, u32[]{:S(2)}, u32[]{:S(2)}) collective-permute-start(bf16[2,9,32,128]{3,2,1,0:T(8,128)(2,1)S(1)} %collective-permute-done.33.refs_4_), channel_id=1, source_target_pairs={{0,1},{1,0},{2,3},{3,2},{4,5},{5,4},{6,7},{7,6},{8,9},{9,8},{10,11... | collective-permute-start | bytes 442376 | tf_op jit(solution)/shard_map/ppermute | solution.py:246
  106.9 1.4 collective-permute-start.41
  106.9 1.6 %collective-permute-start.43 = (bf16[2,9,32,128]{3,2,1,0:T(8,128)(2,1)S(1)}, bf16[2,9,32,128]{3,2,1,0:T(8,128)(2,1)S(1)}, u32[]{:S(2)}, u32[]{:S(2)}) collective-permute-start(bf16[2,9,32,128]{3,2,1,0:T(8,128)(2,1)S(1)} %collective-permute-done.35.refs_5_), channel_id=1, source_target_pairs={{0,1},{1,0},{2,3},{3,2},{4,5},{5,4},{6,7},{7,6},{8,9},{9,8},{10,11... | collective-permute-start | bytes 442376 | tf_op jit(solution)/shard_map/ppermute | solution.py:246
  107.4 1.4 collective-permute-start.44
  107.5 1.5 %collective-permute-start.45 = (bf16[2,9,32,128]{3,2,1,0:T(8,128)(2,1)S(1)}, bf16[2,9,32,128]{3,2,1,0:T(8,128)(2,1)S(1)}, u32[]{:S(2)}, u32[]{:S(2)}) collective-permute-start(bf16[2,9,32,128]{3,2,1,0:T(8,128)(2,1)S(1)} %collective-permute-done.37.refs_7_), channel_id=1, source_target_pairs={{0,1},{1,0},{2,3},{3,2},{4,5},{5,4},{6,7},{7,6},{8,9},{9,8},{10,11... | collective-permute-start | bytes 442376 | tf_op jit(solution)/shard_map/ppermute | solution.py:246
  112.6 4.7 %collective-permute-start.46 = (bf16[4,2,9,32,128]{4,3,2,1,0:T(8,128)(2,1)S(1)}, bf16[4,2,9,32,128]{4,3,2,1,0:T(8,128)(2,1)S(1)}, u32[]{:S(2)}, u32[]{:S(2)}) collective-permute-start(bf16[4,2,9,32,128]{4,3,2,1,0:T(8,128)(2,1)S(1)} %get-tuple-element.199), channel_id=1, source_target_pairs={{0,1},{1,0},{2,3},{3,2},{4,5},{5,4},{6,7},{7,6},{8,9},{9,8},{10,11... | collective-permute-start | bytes 1769480 | tf_op jit(solution)/shard_map/ppermute | solution.py:246
  113.0 4.5 %collective-permute-start.48 = (bf16[1,32,256]{2,1,0:T(8,128)(2,1)S(1)}, bf16[1,32,256]{2,1,0:T(8,128)(2,1)S(1)}, u32[]{:S(2)}, u32[]{:S(2)}) collective-permute-start(bf16[1,32,256]{2,1,0:T(8,128)(2,1)S(1)} %get-tuple-element.205), channel_id=1, source_target_pairs={{2,4},{3,5},{4,2},{5,3},{6,8},{7,9},{8,6},{9,7},{10,12},{11,13},{1... | collective-permute-start | bytes 49160 | tf_op jit(solution)/shard_map/ppermute | solution.py:360
  113.6 5.5 %collective-permute-start.47 = (bf16[1,32,256]{2,1,0:T(8,128)(2,1)S(1)}, bf16[1,32,256]{2,1,0:T(8,128)(2,1)S(1)}, u32[]{:S(2)}, u32[]{:S(2)}) collective-permute-start(bf16[1,32,256]{2,1,0:T(8,128)(2,1)S(1)} %get-tuple-element.205), channel_id=1, source_target_pairs={{0,2},{1,3},{2,0},{3,1},{4,6},{5,7},{6,4},{7,5},{8,10},{9,11},{10,... | collective-permute-start | bytes 49160 | tf_op jit(solution)/shard_map/ppermute | solution.py:360
  119.1 12.3 %collective-permute-start.52 = (bf16[4,2,9,32,128]{4,3,2,1,0:T(8,128)(2,1)S(1)}, bf16[4,2,9,32,128]{4,3,2,1,0:T(8,128)(2,1)S(1)}, u32[]{:S(2)}, u32[]{:S(2)}) collective-permute-start(bf16[4,2,9,32,128]{4,3,2,1,0:T(8,128)(2,1)S(1)} %get-tuple-element.209), channel_id=1, source_target_pairs={{0,1},{1,0},{2,3},{3,2},{4,5},{5,4},{6,7},{7,6},{8,9},{9,8},{10,11... | collective-permute-start | bytes 1769480 | tf_op jit(solution)/shard_map/ppermute | solution.py:246
  119.1 6.0 %collective-permute-start.49 = (bf16[2,9,32,128]{3,2,1,0:T(8,128)(2,1)S(1)}, bf16[2,9,32,128]{3,2,1,0:T(8,128)(2,1)S(1)}, u32[]{:S(2)}, u32[]{:S(2)}) collective-permute-start(bf16[2,9,32,128]{3,2,1,0:T(8,128)(2,1)S(1)} %get-tuple-element.206), channel_id=1, source_target_pairs={{0,4},{1,9},{2,6},{3,11},{4,0},{5,13},{6,2},{7,15},{8,12},{9,1},{1... | collective-permute-start | bytes 442376 | tf_op jit(solution)/shard_map/ppermute | solution.py:241
  121.1 5.2 %collective-permute-start.50 = (bf16[2,9,32,128]{3,2,1,0:T(8,128)(2,1)S(1)}, bf16[2,9,32,128]{3,2,1,0:T(8,128)(2,1)S(1)}, u32[]{:S(2)}, u32[]{:S(2)}) collective-permute-start(bf16[2,9,32,128]{3,2,1,0:T(8,128)(2,1)S(1)} %get-tuple-element.207), channel_id=1, source_target_pairs={{0,8},{1,3},{2,10},{3,1},{4,12},{5,7},{6,14},{7,5},{8,0},{9,11},{1... | collective-permute-start | bytes 442376 | tf_op jit(solution)/shard_map/ppermute | solution.py:241
  123.1 8.3 %collective-permute-start.51 = (bf16[2,9,32,128]{3,2,1,0:T(8,128)(2,1)S(1)}, bf16[2,9,32,128]{3,2,1,0:T(8,128)(2,1)S(1)}, u32[]{:S(2)}, u32[]{:S(2)}) collective-permute-start(bf16[2,9,32,128]{3,2,1,0:T(8,128)(2,1)S(1)} %get-tuple-element.208), channel_id=1, source_target_pairs={{0,2},{1,5},{2,0},{3,7},{4,6},{5,1},{6,4},{7,3},{8,10},{9,13},{10,... | collective-permute-start | bytes 442376 | tf_op jit(solution)/shard_map/ppermute | solution.py:241
  125.1 12.2 %collective-permute-start.56 = (bf16[2,9,32,128]{3,2,1,0:T(8,128)(2,1)S(1)}, bf16[2,9,32,128]{3,2,1,0:T(8,128)(2,1)S(1)}, u32[]{:S(2)}, u32[]{:S(2)}) collective-permute-start(bf16[2,9,32,128]{3,2,1,0:T(8,128)(2,1)S(1)} %get-tuple-element.225), channel_id=1, source_target_pairs={{0,14},{1,15},{2,12},{3,13},{4,10},{5,11},{6,8},{7,9},{8,6},{9,7},... | collective-permute-start | bytes 442376 | tf_op jit(solution)/shard_map/ppermute | solution.py:241
  131.6 6.1 %collective-permute-start.53 = (bf16[2,9,32,128]{3,2,1,0:T(8,128)(2,1)S(1)}, bf16[2,9,32,128]{3,2,1,0:T(8,128)(2,1)S(1)}, u32[]{:S(2)}, u32[]{:S(2)}) collective-permute-start(bf16[2,9,32,128]{3,2,1,0:T(8,128)(2,1)S(1)} %get-tuple-element.222), channel_id=1, source_target_pairs={{0,2},{1,5},{2,0},{3,7},{4,6},{5,1},{6,4},{7,3},{8,10},{9,13},{10,... | collective-permute-start | bytes 442376 | tf_op jit(solution)/shard_map/ppermute | solution.py:241
  133.3 5.1 %collective-permute-start.54 = (bf16[2,9,32,128]{3,2,1,0:T(8,128)(2,1)S(1)}, bf16[2,9,32,128]{3,2,1,0:T(8,128)(2,1)S(1)}, u32[]{:S(2)}, u32[]{:S(2)}) collective-permute-start(bf16[2,9,32,128]{3,2,1,0:T(8,128)(2,1)S(1)} %get-tuple-element.223), channel_id=1, source_target_pairs={{0,4},{1,9},{2,6},{3,11},{4,0},{5,13},{6,2},{7,15},{8,12},{9,1},{1... | collective-permute-start | bytes 442376 | tf_op jit(solution)/shard_map/ppermute | solution.py:241
  134.5 5.1 %collective-permute-start.55 = (bf16[2,9,32,128]{3,2,1,0:T(8,128)(2,1)S(1)}, bf16[2,9,32,128]{3,2,1,0:T(8,128)(2,1)S(1)}, u32[]{:S(2)}, u32[]{:S(2)}) collective-permute-start(bf16[2,9,32,128]{3,2,1,0:T(8,128)(2,1)S(1)} %get-tuple-element.224), channel_id=1, source_target_pairs={{0,8},{1,3},{2,10},{3,1},{4,12},{5,7},{6,14},{7,5},{8,0},{9,11},{1... | collective-permute-start | bytes 442376 | tf_op jit(solution)/shard_map/ppermute | solution.py:241
  134.8 1.2 collective-permute-start.57
  136.0 1.2 collective-permute-start.58
  139.7 5.9 %collective-permute-start.59 = (bf16[9,32,128]{2,1,0:T(8,128)(2,1)S(1)}, bf16[9,32,128]{2,1,0:T(8,128)(2,1)S(1)}, u32[]{:S(2)}, u32[]{:S(2)}) collective-permute-start(bf16[9,32,128]{2,1,0:T(8,128)(2,1)S(1)} %get-tuple-element.235), channel_id=1, source_target_pairs={{0,16},{1,17},{2,18},{3,19},{4,20},{5,21},{6,22},{7,23},{8,24},{9,... | collective-permute-start | bytes 221192 | tf_op jit(solution)/shard_map/ppermute | solution.py:237
  (20 other events, 89.4 us)

commit v14 on v13

--- a/solution.py
+++ b/solution.py
@@ -2,12 +2,14 @@
 
 import jax
 import jax.numpy as jnp
+import numpy as np
 from jax import lax
 from jax.experimental import pallas as pl
 from jax.experimental.pallas import tpu as pltpu
 from jax.sharding import PartitionSpec as P
 
 LANES = 128
+CORES, CHIPS = 2, 8
 BF = jnp.bfloat16
 F32 = jnp.float32
 VMEM = pl.BlockSpec(memory_space=pltpu.VMEM)
@@ -69,20 +71,20 @@
     return copies
 
 
-def emit_edges(core_ref, v_ref, inner_ref, outer_ref):
+def emit_edges(v_ref, inner_ref, outer_ref):
     head, tail = v_ref[0], v_ref[v_ref.shape[0] - 1]
-    even = core_ref[0] == 0
+    even = lax.axis_index("clu") % CORES == 0
     inner_ref[0] = jnp.where(even, tail, head)
     outer_ref[0] = jnp.where(even, head, tail)
 
 
 def coeff_kernel(
-    ranks_ref, core_ref, v_hbm, basis_hbm, transfer_hbm, out_ref, inner_ref, outer_ref, v_ref, basis_ref, transfer_ref, sems
+    ranks_ref, v_hbm, basis_hbm, transfer_hbm, out_ref, inner_ref, outer_ref, v_ref, basis_ref, transfer_ref, sems
 ):
     leaves, rank_top, _ = basis_ref.shape
     for copy in fetch([(v_hbm, v_ref), (basis_hbm, basis_ref), (transfer_hbm, transfer_ref)], sems):
         copy.wait()
-    emit_edges(core_ref, v_ref, inner_ref, outer_ref)
+    emit_edges(v_ref, inner_ref, outer_ref)
     emit_coeffs(lambda i: v_ref[i], basis_ref, transfer_ref, ranks_ref, out_ref, leaves, rank_top)
 
 
@@ -133,7 +135,7 @@
     lax.fori_loop(0, far, pack, 0)
 
 
-def near_kernel(v_ref, near_ref, _, out_ref):
+def near_kernel(v_ref, near_ref, out_ref):
     leaves = v_ref.shape[0]
     for i in range(leaves):
         total = dot(v_ref[i], near_ref[i, 1])
@@ -144,9 +146,9 @@
         out_ref[i] = total
 
 
-def edge_kernel(core_ref, inner_ref, outer_ref, first_ref, last_ref, out_ref):
+def edge_kernel(inner_ref, outer_ref, first_ref, last_ref, out_ref):
     inner, outer = inner_ref[0], outer_ref[0]
-    even = core_ref[0] == 0
+    even = lax.axis_index("clu") % CORES == 0
     out_ref[0] = dot(jnp.where(even, outer, inner), first_ref[0, 0])
     out_ref[1] = dot(jnp.where(even, inner, outer), last_ref[0, 0])
 
@@ -164,8 +166,23 @@
         out_ref[...] = (total + part_ref[...].astype(F32)).astype(BF)
 
 
-def pick_kernel(flag_ref, first_ref, second_ref, out_ref):
-    out_ref[...] = jnp.where(flag_ref[0] == 0, first_ref[...], second_ref[...])
+def pick_kernel(even_ref, odd_ref, out_ref):
+    me, devices = lax.axis_index("clu"), lax.axis_size("clu")
+    row = jnp.where((me // CORES + me % CORES) % 2 == 0, even_ref[...], odd_ref[...])
+    inside = (me != CORES - 1) & (me != devices - CORES)
+    out_ref[...] = jnp.where(inside, row, jnp.zeros_like(row))
+
+
+def rows_kernel(source_ref, target_ref, source_out, target_out, *, clusters, far, magic, shift):
+    me = lax.axis_index("clu")
+    for sign, in_ref, out_ref in ((-1, source_ref, source_out), (1, target_ref, target_out)):
+        cluster = in_ref[...]
+        device = cluster * magic >> shift
+        chip = ((device ^ me) >> 1) & (CHIPS - 1)
+        chip = jnp.where((device & 1) == 0, chip, chip >> 1 | (chip & 1) << 2)
+        away = (sign * ((device >> 4) - (me >> 4))) & (far - 1)
+        core = (device ^ me) & 1
+        out_ref[...] = ((core * CHIPS + chip) * far + away) * clusters + cluster - device * clusters
 
 
 def join_kernel(*refs):
@@ -185,7 +202,7 @@
             away_refs[f - 1][...] = total.astype(BF)
 
 
-def field_kernel(ranks_ref, core_ref, near_ref, edge_ref, basis_ref, transfer_ref, keep_ref, *rest, away):
+def field_kernel(ranks_ref, near_ref, edge_ref, basis_ref, transfer_ref, keep_ref, *rest, away):
     term_refs, out_ref, next_refs = rest[:away], rest[away], rest[away + 1 :]
     leaves, rank_top, _ = basis_ref.shape
     mains, rhs, _ = keep_ref.shape
@@ -211,7 +228,7 @@
         out_ref[i] = result.astype(BF)
     if next_refs:
         coeff_ref, inner_ref, outer_ref = next_refs
-        emit_edges(core_ref, out_ref, inner_ref, outer_ref)
+        emit_edges(out_ref, inner_ref, outer_ref)
         emit_coeffs(lambda i: out_ref[i], basis_ref, transfer_ref, ranks_ref, coeff_ref, leaves, rank_top)
 
 
@@ -228,7 +245,7 @@
     mains = clusters * 3 // 4
     shape = jax.ShapeDtypeStruct
 
-    cores, chips = 2, 8
+    cores, chips = CORES, CHIPS
     cube = cores * chips
     far = devices // cube
     x, y, z = 1, 2, 4
@@ -245,30 +262,31 @@
     def swap_cores(part):
         return lax.ppermute(part, "clu", [(d, d ^ 1) for d in range(devices)])
 
-    me = lax.axis_index("clu")
-    core = me % cores
     barrier = lax.optimization_barrier
 
-    def rows(cluster, sign):
-        device = cluster // clusters
-        core = (device ^ me) % cores
-        chip = ((device ^ me) // cores) % chips
-        chip = jnp.where(device % cores == 0, chip, chip >> 1 | (chip & 1) << 2)
-        away = (sign * (device // cube - me // cube)) % far
-        return ((core * chips + chip) * far + away) * clusters + cluster % clusters
-
-    source_rows, target_rows = rows(block_source, -1), rows(block_target, 1)
+    shift = 19
+    magic = -(-(1 << shift) // clusters)
+    numbers = np.arange(devices * clusters)
+    assert (numbers * magic >> shift == numbers // clusters).all() and far & far - 1 == 0
+    list_shape = jax.ShapeDtypeStruct((1, blocks), jnp.int32)
+    source_rows, target_rows = pl.pallas_call(
+        functools.partial(rows_kernel, clusters=clusters, far=far, magic=magic, shift=shift),
+        out_shape=[list_shape] * 2,
+        in_specs=[VMEM] * 2,
+        out_specs=[VMEM] * 2,
+        compiler_params=params(1),
+    )(block_source.reshape(1, blocks), block_target.reshape(1, blocks))
+    source_rows, target_rows = source_rows.reshape(blocks), target_rows.reshape(blocks)
 
     tile_shape = (mains, rhs, LANES)
     out_shape = shape((leaves, rhs, width), BF)
     tile_out = shape(tile_shape, BF)
     part_shape = shape((far,) + tile_shape, BF)
     edge_shape = shape((1, rhs, width), BF)
-    core_index = core.reshape(1)
     first_coeffs, inner, outer = pl.pallas_call(
         coeff_kernel,
         out_shape=[tile_out, edge_shape, edge_shape],
-        in_specs=[SMEM, SMEM, HBM, HBM, HBM],
+        in_specs=[SMEM, HBM, HBM, HBM],
         out_specs=[VMEM] * 3,
         scratch_shapes=[
             pltpu.VMEM(charges.shape, BF),
@@ -276,7 +294,7 @@
             pltpu.VMEM(transfer.shape, BF),
             pltpu.SemaphoreType.DMA((3,)),
         ],
-    )(ranks, core_index, charges, basis, transfer)
+    )(ranks, charges, basis, transfer)
 
     order = ((x | y | z, x | y, y | z, z | x), (0, x, y, z))
     couple = pl.pallas_call(
@@ -297,7 +315,7 @@
     near = pl.pallas_call(
         near_kernel,
         out_shape=shape((leaves, rhs, width), F32),
-        in_specs=[VMEM, VMEM, pl.BlockSpec(memory_space=pl.ANY)],
+        in_specs=[VMEM, VMEM],
         out_specs=VMEM,
         compiler_params=params(16),
         cost_estimate=pl.CostEstimate(
@@ -310,7 +328,6 @@
         out_shape=shape((2, rhs, width), F32),
         grid=(1,),
         in_specs=[
-            SMEM,
             VMEM,
             VMEM,
             pl.BlockSpec((1, 1, width, width), lambda i: (0, 0, 0, 0)),
@@ -331,6 +348,12 @@
 
     own_shape = shape((far,) + tile_shape, F32)
     join = adder(join_kernel, far, [part_shape])
+    first_join = pl.pallas_call(
+        lambda _, *refs: join_kernel(*refs),
+        out_shape=[part_shape],
+        in_specs=[pl.BlockSpec(memory_space=pl.ANY)] + [VMEM] * far,
+        out_specs=[VMEM],
+    )
     far_add = adder(add_kernel, 2, [part_shape] * 4)
     middle_add = adder(functools.partial(middle_add_kernel, parts=3), 5, [own_shape] + [part_shape] * 3)
     last_add = adder(
@@ -341,7 +364,7 @@
         return pl.pallas_call(
             functools.partial(field_kernel, away=far - 1),
             out_shape=[out_shape, tile_out, edge_shape, edge_shape] if with_coeffs else [out_shape],
-            in_specs=[SMEM, SMEM] + [VMEM] * (4 + far),
+            in_specs=[SMEM] + [VMEM] * (4 + far),
             out_specs=[VMEM] * 4 if with_coeffs else [VMEM],
             compiler_params=params(16),
         )
@@ -350,19 +373,21 @@
     halo_pairs = []
     for parity in range(2):
         chain = [(c, c + 1) for c in range(parity, count - 1, 2)]
-        halo_pairs.append([(a * cores + k, b * cores + k) for p in chain for a, b in (p, p[::-1]) for k in range(cores)])
-    halo_turn = ((me // cores + core) % 2).reshape(1)
+        ends = [(c, c) for c in (0, count - 1) if parity]
+        links = [link for pair in chain for link in (pair, pair[::-1])] + ends
+        halo_pairs.append([(a * cores + k, b * cores + k) for a, b in links for k in range(cores)])
     pick = pl.pallas_call(
-        pick_kernel, out_shape=edge_shape, in_specs=[SMEM, VMEM, VMEM], out_specs=VMEM, compiler_params=params(1)
+        pick_kernel, out_shape=edge_shape, in_specs=[VMEM, VMEM], out_specs=VMEM, compiler_params=params(1)
     )
 
     def swap_halo(edge_row):
         return [lax.ppermute(edge_row, "clu", pairs) for pairs in halo_pairs]
 
     def apply_matrix(field_in, coeffs, inner, outer, coupling, with_coeffs):
-        (column,) = join(coeffs, *[swap_far(coeffs, s) for s in range(1, far)])
+        away = [swap_far(coeffs, s) for s in range(1, far)]
+        (column,) = first_join(coupling, coeffs, *away) if with_coeffs else join(coeffs, *away)
         got = {0: column, x: swap(column, x), y: swap(column, y), z: swap(column, z)}
-        near_sum = near(field_in, near_field, coupling)
+        near_sum = near(field_in, near_field)
         got, near_sum = barrier((got, near_sum))
         corner = swap(column, x | y | z)
         other = {chip: swap_cores(part) for chip, part in got.items()}
@@ -382,15 +407,15 @@
         corner, xy, yz, zx, send, outer = barrier((corner, xy, yz, zx, send, swap_halo(outer)))
         to_x, to_y, to_z, swapped = barrier((swap(xy, y), swap(yz, z), swap(zx, x), swap_cores(send)))
         own, to_x, to_y, to_z, inner, outer = barrier(
-            (*middle_add(keep, swapped, to_x, to_y, to_z), inner, pick(halo_turn, *outer))
-        )
-        edges = edge(core_index, swap_cores(inner), swap_cores(outer), near_field, near_field)
+            (*middle_add(keep, swapped, to_x, to_y, to_z), inner, pick(*outer))
+        )
+        edges = edge(swap_cores(inner), swap_cores(outer), near_field, near_field)
         own, to_x, to_y, to_z, corner, edges = barrier(
             (own, swap(to_x, x), swap(to_y, y), swap(to_z, z), swap(corner, x | y | z), edges)
         )
         total, *away = last_add(own, to_x, to_y, to_z, corner)
         terms = [swap_far(part, s + 1) for s, part in enumerate(away)]
-        return finish(with_coeffs)(ranks, core_index, near_sum, edges, basis, transfer, total, *terms)
+        return finish(with_coeffs)(ranks, near_sum, edges, basis, transfer, total, *terms)
 
     first, *second_args = apply_matrix(charges, first_coeffs, inner, outer, coupling, True)
     (second,) = apply_matrix(first, *second_args, coupling, False)

time: 149 us -> 137 us (0.919)
  local copies, waits for them, and re-layouts: 18.1 us -> 6.37 us
  waiting for transfers between devices: 53 us -> 55.8 us
  Pallas kernels: 21.2 us -> 19 us
    unnamed x49 -> x27, local copies, waits for them, and re-layouts: 18.1 us -> 6.37 us
    ppermute x28, waiting for transfers between devices: 25.7 us -> 30.6 us  [swap(): lax.ppermute(part, 'clu', [(d, d ^ (turned if d % cores else direction) *...]
    ppermute x4, waiting for transfers between devices: 18.6 us -> 15 us  [swap_far(): lax.ppermute(part, 'clu', [(d, (d + shift * cube) % devices) for d in ran...]
    pallas_call x2, Pallas kernels: 8.92 us -> 7.21 us  [apply_matrix(): couple(source_rows, target_rows, coupling, *[got[chip] for chip in range(...]
    ppermute x4, waiting for transfers between devices: 1.66 us -> 3.3 us  [swap_halo(): return [lax.ppermute(edge_row, 'clu', pairs) for pairs in halo_pairs]]
    pallas_call x10 -> x11, Pallas kernels: 6.48 us -> 8.1 us  [the longest x2 4.98 us: apply_matrix(): finish(with_coeffs)(ranks, near_sum, edges, basis, transfer, total, *terms)]
  transfers between devices with their start and end apart: 60 -> 60, of which waited for: 33 -> 38; matrix products, arithmetic and copies ran while one was open for 4% -> 4% of each run, Pallas kernels for 3% -> 2%
where the time goes in v14:
time: 137 us; the launch traced here: 136 us
  waiting for transfers between devices  55.8 us (41%)
  starting transfers between devices  54.2 us (40%)
  Pallas kernels  19 us (14%)
  local copies, waits for them, and re-layouts  6.37 us (5%)
    ppermute x28, starting transfers between devices, swap(): lax.ppermute(part, 'clu', [(d, d ^ (turned if d % cores else direction) *...  34 us
    ppermute x28, waiting for transfers between devices, swap(): lax.ppermute(part, 'clu', [(d, d ^ (turned if d % cores else direction) *...  30.6 us
    ppermute x4, waiting for transfers between devices, swap_far(): lax.ppermute(part, 'clu', [(d, (d + shift * cube) % devices) for d in ran...  15 us
    ppermute x4, starting transfers between devices, swap_halo(): return [lax.ppermute(edge_row, 'clu', pairs) for pairs in halo_pairs]  9.78 us
    pallas_call x2, Pallas kernels, apply_matrix(): couple(source_rows, target_rows, coupling, *[got[chip] for chip in range(...  7.21 us
    ppermute x24, waiting for transfers between devices, swap_cores(): return lax.ppermute(part, 'clu', [(d, d ^ 1) for d in range(devices)])  6.91 us
    unnamed x27, local copies, waits for them, and re-layouts  6.37 us
    ppermute x4, starting transfers between devices, swap_far(): lax.ppermute(part, 'clu', [(d, (d + shift * cube) % devices) for d in ran...  6.16 us
  transfers between devices with their start and end apart: 60, of which 38 were waited for; matrix products, arithmetic and copies ran while one was open for 4% of the time, Pallas kernels for 2%

profile of v14, /device:TPU:0, one launch (start us, length us, event | category | flops | bytes accessed | tf_op | source)
XLA Modules:
  0.0 136.3 jit_solution(2114717359010777388)
XLA Ops:
  0.6 2.9 %shard_map.95 = (bf16[9,32,128]{2,1,0:T(8,128)(2,1)}, bf16[1,32,256]{2,1,0:T(8,128)(2,1)}, bf16[1,32,256]{2,1,0:T(8,128)(2,1)}) custom-call(s32[12]{0:T(128)} %ranks_ref.5, bf16[8,32,256]{2,1,0:T(8,128)(2,1)} %v_ref.1, bf16[8,96,256]{2,1,0:T(8,128)(2,1)} %basis_ref.3, bf16[8,96,96]{2,1,0:T(8,128)(2,1)} %transfer_ref.3), custom_call_target="tpu_custom_call" | custom-call | tf_op jit(solution)/shard_map/pallas_call | solution.py:286
  3.6 4.1 %collective-permute-start = (bf16[9,32,128]{2,1,0:T(8,128)(2,1)}, bf16[9,32,128]{2,1,0:T(8,128)(2,1)S(1)}, u32[]{:S(2)}, u32[]{:S(2)}) collective-permute-start(bf16[9,32,128]{2,1,0:T(8,128)(2,1)} %get-tuple-element.121.refs_0_), channel_id=1, source_target_pairs={{0,16},{1,17},{2,18},{3,19},{4,20},{5,21},{6,22},{7,23},{8,24},{9,... | collective-permute-start | bytes 221192 | tf_op jit(solution)/shard_map/ppermute | solution.py:254
  7.7 4.8 %copy.10._.coupling_ref = bf16[128,96,96]{2,1,0:T(8,128)(2,1)} copy(bf16[128,96,96]{0,2,1:T(8,128)(2,1)} %param.12) | data formatting | bytes 4718592 | tf_op args[4]
  12.5 0.6 copy-done.10
  13.1 1.6 %shard_map.96.refs_0_ = bf16[2,9,32,128]{3,2,1,0:T(8,128)(2,1)} custom-call(bf16[128,96,96]{2,1,0:T(8,128)(2,1)} %copy.10._.coupling_ref, bf16[9,32,128]{2,1,0:T(8,128)(2,1)} %get-tuple-element.121.refs_0_, bf16[9,32,128]{2,1,0:T(8,128)(2,1)} %copy-done.10), custom_call_target="tpu_custom_call" | custom-call | tf_op jit(solution)/shard_map/pallas_call | solution.py:388
  14.7 1.6 %collective-permute-start.3 = (bf16[2,9,32,128]{3,2,1,0:T(8,128)(2,1)}, bf16[2,9,32,128]{3,2,1,0:T(8,128)(2,1)S(1)}, u32[]{:S(2)}, u32[]{:S(2)}) collective-permute-start(bf16[2,9,32,128]{3,2,1,0:T(8,128)(2,1)} %shard_map.96.refs_0_), channel_id=1, source_target_pairs={{0,8},{1,3},{2,10},{3,1},{4,12},{5,7},{6,14},{7,5},{8,0},{9,11},{1... | collective-permute-start | bytes 442376 | tf_op jit(solution)/shard_map/ppermute | solution.py:258
  16.3 1.5 %collective-permute-start.2 = (bf16[2,9,32,128]{3,2,1,0:T(8,128)(2,1)}, bf16[2,9,32,128]{3,2,1,0:T(8,128)(2,1)S(1)}, u32[]{:S(2)}, u32[]{:S(2)}) collective-permute-start(bf16[2,9,32,128]{3,2,1,0:T(8,128)(2,1)} %shard_map.96.refs_0_), channel_id=1, source_target_pairs={{0,4},{1,9},{2,6},{3,11},{4,0},{5,13},{6,2},{7,15},{8,12},{9,1},{1... | collective-permute-start | bytes 442376 | tf_op jit(solution)/shard_map/ppermute | solution.py:258
  17.8 1.5 %collective-permute-start.1 = (bf16[2,9,32,128]{3,2,1,0:T(8,128)(2,1)}, bf16[2,9,32,128]{3,2,1,0:T(8,128)(2,1)S(1)}, u32[]{:S(2)}, u32[]{:S(2)}) collective-permute-start(bf16[2,9,32,128]{3,2,1,0:T(8,128)(2,1)} %shard_map.96.refs_0_), channel_id=1, source_target_pairs={{0,2},{1,5},{2,0},{3,7},{4,6},{5,1},{6,4},{7,3},{8,10},{9,13},{10,... | collective-permute-start | bytes 442376 | tf_op jit(solution)/shard_map/ppermute | solution.py:258
  19.3 0.6 shard_map.97.near_ref
  20.3 1.3 collective-permute-done.3.refs_4_
  21.6 1.9 %collective-permute-done.2.refs_2_ = bf16[2,9,32,128]{3,2,1,0:T(8,128)(2,1)S(1)} collective-permute-done((bf16[2,9,32,128]{3,2,1,0:T(8,128)(2,1)}, bf16[2,9,32,128]{3,2,1,0:T(8,128)(2,1)S(1)}, u32[]{:S(2)}, u32[]{:S(2)}) %collective-permute-start.2) | collective-permute-done | bytes 147488 | tf_op jit(solution)/shard_map/ppermute | solution.py:258
  23.5 2.8 %collective-permute-done.1.refs_1_ = bf16[2,9,32,128]{3,2,1,0:T(8,128)(2,1)S(1)} collective-permute-done((bf16[2,9,32,128]{3,2,1,0:T(8,128)(2,1)}, bf16[2,9,32,128]{3,2,1,0:T(8,128)(2,1)S(1)}, u32[]{:S(2)}, u32[]{:S(2)}) %collective-permute-start.1) | collective-permute-done | bytes 147488 | tf_op jit(solution)/shard_map/ppermute | solution.py:258
  26.3 2.4 %collective-permute-start.5 = (bf16[2,9,32,128]{3,2,1,0:T(8,128)(2,1)S(1)}, bf16[2,9,32,128]{3,2,1,0:T(8,128)(2,1)S(1)}, u32[]{:S(2)}, u32[]{:S(2)}) collective-permute-start(bf16[2,9,32,128]{3,2,1,0:T(8,128)(2,1)S(1)} %collective-permute-done.3.refs_4_), channel_id=1, source_target_pairs={{0,2},{1,5},{2,0},{3,7},{4,6},{5,1},{6,4},{7,3},{8,10},{9,13},{10,... | collective-permute-start | bytes 442376 | tf_op jit(solution)/shard_map/ppermute | solution.py:258
  29.2 2.2 %collective-permute-done.4.refs_3_ = bf16[2,9,32,128]{3,2,1,0:T(8,128)(2,1)S(1)} collective-permute-done((bf16[2,9,32,128]{3,2,1,0:T(8,128)(2,1)S(1)}, bf16[2,9,32,128]{3,2,1,0:T(8,128)(2,1)S(1)}, u32[]{:S(2)}, u32[]{:S(2)}) %collective-permute-start.4) | collective-permute-done | bytes 147488 | tf_op jit(solution)/shard_map/ppermute | solution.py:258
  34.1 3.6 %shard_map.99 = (bf16[4,2,9,32,128]{4,3,2,1,0:T(8,128)(2,1)S(1)}, bf16[4,2,9,32,128]{4,3,2,1,0:T(8,128)(2,1)S(1)}, bf16[4,2,9,32,128]{4,3,2,1,0:T(8,128)(2,1)S(1)}, bf16[4,2,9,32,128]{4,3,2,1,0:T(8,128)(2,1)S(1)}) custom-call(s32[128]{0:T(128)S(1)} %bitcast.4, s32[128]{0:T(128)S(1)} %bitcast.6, bf16[128,96,96]{2,1,0:T(8,128)(2,1)S(1)} %copy-done.1, ...), custom_call_target="tpu_custom_call" | custom-call | flops 75497472 | bytes 10485760 | tf_op jit(solution)/shard_map/pallas_call | solution.py:398
  38.0 0.7 collective-permute-start.18
  38.6 4.7 %collective-permute-start.17 = (bf16[1,32,256]{2,1,0:T(8,128)(2,1)S(1)}, bf16[1,32,256]{2,1,0:T(8,128)(2,1)S(1)}, u32[]{:S(2)}, u32[]{:S(2)}) collective-permute-start(bf16[1,32,256]{2,1,0:T(8,128)(2,1)S(1)} %copy-done.12), channel_id=1, source_target_pairs={{0,2},{1,3},{2,0},{3,1},{4,6},{5,7},{6,4},{7,5},{8,10},{9,11},{10,... | collective-permute-start | bytes 49160 | tf_op jit(solution)/shard_map/ppermute | solution.py:384
  43.5 1.6 %collective-permute-done.17.even_ref = bf16[1,32,256]{2,1,0:T(8,128)(2,1)S(1)} collective-permute-done((bf16[1,32,256]{2,1,0:T(8,128)(2,1)S(1)}, bf16[1,32,256]{2,1,0:T(8,128)(2,1)S(1)}, u32[]{:S(2)}, u32[]{:S(2)}) %collective-permute-start.17) | collective-permute-done | bytes 16416 | tf_op jit(solution)/shard_map/ppermute | solution.py:384
  45.2 2.4 %collective-permute-start.19 = (bf16[2,9,32,128]{3,2,1,0:T(8,128)(2,1)S(1)}, bf16[2,9,32,128]{3,2,1,0:T(8,128)(2,1)S(1)}, u32[]{:S(2)}, u32[]{:S(2)}) collective-permute-start(bf16[2,9,32,128]{3,2,1,0:T(8,128)(2,1)S(1)} %get-tuple-element.151), channel_id=1, source_target_pairs={{0,4},{1,9},{2,6},{3,11},{4,0},{5,13},{6,2},{7,15},{8,12},{9,1},{1... | collective-permute-start | bytes 442376 | tf_op jit(solution)/shard_map/ppermute | solution.py:258
  47.5 1.5 %collective-permute-start.20 = (bf16[2,9,32,128]{3,2,1,0:T(8,128)(2,1)S(1)}, bf16[2,9,32,128]{3,2,1,0:T(8,128)(2,1)S(1)}, u32[]{:S(2)}, u32[]{:S(2)}) collective-permute-start(bf16[2,9,32,128]{3,2,1,0:T(8,128)(2,1)S(1)} %get-tuple-element.152), channel_id=1, source_target_pairs={{0,8},{1,3},{2,10},{3,1},{4,12},{5,7},{6,14},{7,5},{8,0},{9,11},{1... | collective-permute-start | bytes 442376 | tf_op jit(solution)/shard_map/ppermute | solution.py:258
  49.0 2.3 %collective-permute-start.21 = (bf16[2,9,32,128]{3,2,1,0:T(8,128)(2,1)S(1)}, bf16[2,9,32,128]{3,2,1,0:T(8,128)(2,1)S(1)}, u32[]{:S(2)}, u32[]{:S(2)}) collective-permute-start(bf16[2,9,32,128]{3,2,1,0:T(8,128)(2,1)S(1)} %get-tuple-element.153), channel_id=1, source_target_pairs={{0,2},{1,5},{2,0},{3,7},{4,6},{5,1},{6,4},{7,3},{8,10},{9,13},{10,... | collective-permute-start | bytes 442376 | tf_op jit(solution)/shard_map/ppermute | solution.py:258
  51.6 1.6 %collective-permute-done.20.refs_1_ = bf16[2,9,32,128]{3,2,1,0:T(8,128)(2,1)S(1)} collective-permute-done((bf16[2,9,32,128]{3,2,1,0:T(8,128)(2,1)S(1)}, bf16[2,9,32,128]{3,2,1,0:T(8,128)(2,1)S(1)}, u32[]{:S(2)}, u32[]{:S(2)}) %collective-permute-start.20) | collective-permute-done | bytes 147488 | tf_op jit(solution)/shard_map/ppermute | solution.py:258
  53.2 4.6 %collective-permute-done.21.refs_2_ = bf16[2,9,32,128]{3,2,1,0:T(8,128)(2,1)S(1)} collective-permute-done((bf16[2,9,32,128]{3,2,1,0:T(8,128)(2,1)S(1)}, bf16[2,9,32,128]{3,2,1,0:T(8,128)(2,1)S(1)}, u32[]{:S(2)}, u32[]{:S(2)}) %collective-permute-start.21) | collective-permute-done | bytes 147488 | tf_op jit(solution)/shard_map/ppermute | solution.py:258
  58.1 1.9 %collective-permute-start.23 = (bf16[2,9,32,128]{3,2,1,0:T(8,128)(2,1)S(1)}, bf16[2,9,32,128]{3,2,1,0:T(8,128)(2,1)S(1)}, u32[]{:S(2)}, u32[]{:S(2)}) collective-permute-start(bf16[2,9,32,128]{3,2,1,0:T(8,128)(2,1)S(1)} %get-tuple-element.167), channel_id=1, source_target_pairs={{0,2},{1,5},{2,0},{3,7},{4,6},{5,1},{6,4},{7,3},{8,10},{9,13},{10,... | collective-permute-start | bytes 442376 | tf_op jit(solution)/shard_map/ppermute | solution.py:258
  59.9 0.9 collective-permute-start.24
  61.0 1.2 collective-permute-done.27.inner_ref
  62.4 1.0 collective-permute-done.28.outer_ref
  63.8 1.2 collective-permute-done.24.refs_1_
  65.1 0.9 collective-permute-done.25.refs_2_
  66.0 0.5 collective-permute-start.29
  66.5 5.3 %collective-permute-done.29.rest_0_ = bf16[9,32,128]{2,1,0:T(8,128)(2,1)S(1)} collective-permute-done((bf16[9,32,128]{2,1,0:T(8,128)(2,1)S(1)}, bf16[9,32,128]{2,1,0:T(8,128)(2,1)S(1)}, u32[]{:S(2)}, u32[]{:S(2)}) %collective-permute-start.29) | collective-permute-done | bytes 73760 | tf_op jit(solution)/shard_map/ppermute | solution.py:254
  71.8 2.5 %shard_map.105 = (bf16[8,32,256]{2,1,0:T(8,128)(2,1)}, bf16[9,32,128]{2,1,0:T(8,128)(2,1)S(1)}, bf16[1,32,256]{2,1,0:T(8,128)(2,1)S(1)}, bf16[1,32,256]{2,1,0:T(8,128)(2,1)S(1)}) custom-call(s32[12]{0:T(128)S(1)} %copy-done.7, f32[8,32,256]{2,1,0:T(8,128)S(1)} %shard_map.97.near_ref, f32[2,32,256]{2,1,0:T(8,128)S(1)} %shard_map.103.edge_ref, ...), custom_call_target="tpu_custom_call" | custom-call | tf_op jit(solution)/shard_map/pallas_call | solution.py:418
  74.4 5.4 %collective-permute-done.30.refs_1_ = bf16[9,32,128]{2,1,0:T(8,128)(2,1)S(1)} collective-permute-done((bf16[9,32,128]{2,1,0:T(8,128)(2,1)S(1)}, bf16[9,32,128]{2,1,0:T(8,128)(2,1)S(1)}, u32[]{:S(2)}, u32[]{:S(2)}) %collective-permute-start.30) | collective-permute-done | bytes 73760 | tf_op jit(solution)/shard_map/ppermute | solution.py:254
  79.8 1.2 collective-permute-start.32
  81.0 1.1 collective-permute-start.31
  82.1 0.9 copy-done.6
  83.0 0.6 shard_map.107.near_ref
  83.6 2.7 %collective-permute-start.37 = (bf16[2,9,32,128]{3,2,1,0:T(8,128)(2,1)S(1)}, bf16[2,9,32,128]{3,2,1,0:T(8,128)(2,1)S(1)}, u32[]{:S(2)}, u32[]{:S(2)}) collective-permute-start(bf16[2,9,32,128]{3,2,1,0:T(8,128)(2,1)S(1)} %shard_map.106.refs_0_), channel_id=1, source_target_pairs={{0,14},{1,15},{2,12},{3,13},{4,10},{5,11},{6,8},{7,9},{8,6},{9,7},... | collective-permute-start | bytes 442376 | tf_op jit(solution)/shard_map/ppermute | solution.py:258
  86.5 1.0 collective-permute-done.32.refs_2_
  87.5 0.6 collective-permute-done.31.refs_1_
  88.2 1.1 collective-permute-start.34
  89.3 0.8 collective-permute-start.36
  90.1 1.1 collective-permute-start.35
  91.7 1.6 %collective-permute-done.34.refs_3_ = bf16[2,9,32,128]{3,2,1,0:T(8,128)(2,1)S(1)} collective-permute-done((bf16[2,9,32,128]{3,2,1,0:T(8,128)(2,1)S(1)}, bf16[2,9,32,128]{3,2,1,0:T(8,128)(2,1)S(1)}, u32[]{:S(2)}, u32[]{:S(2)}) %collective-permute-start.34) | collective-permute-done | bytes 147488 | tf_op jit(solution)/shard_map/ppermute | solution.py:258
  93.3 1.1 collective-permute-done.36.refs_6_
  94.4 0.8 collective-permute-done.35.refs_5_
  97.3 3.6 %shard_map.108 = (bf16[4,2,9,32,128]{4,3,2,1,0:T(8,128)(2,1)S(1)}, bf16[4,2,9,32,128]{4,3,2,1,0:T(8,128)(2,1)S(1)}, bf16[4,2,9,32,128]{4,3,2,1,0:T(8,128)(2,1)S(1)}, bf16[4,2,9,32,128]{4,3,2,1,0:T(8,128)(2,1)S(1)}) custom-call(s32[128]{0:T(128)S(1)} %bitcast.5, s32[128]{0:T(128)S(1)} %bitcast.7, bf16[128,96,96]{2,1,0:T(8,128)(2,1)S(1)} %copy-done.1, ...), custom_call_target="tpu_custom_call" | custom-call | flops 75497472 | bytes 10485760 | tf_op jit(solution)/shard_map/pallas_call | solution.py:398
  101.3 0.7 collective-permute-start.48
  102.0 3.8 %collective-permute-start.47 = (bf16[1,32,256]{2,1,0:T(8,128)(2,1)S(1)}, bf16[1,32,256]{2,1,0:T(8,128)(2,1)S(1)}, u32[]{:S(2)}, u32[]{:S(2)}) collective-permute-start(bf16[1,32,256]{2,1,0:T(8,128)(2,1)S(1)} %get-tuple-element.209), channel_id=1, source_target_pairs={{0,2},{1,3},{2,0},{3,1},{4,6},{5,7},{6,4},{7,5},{8,10},{9,11},{10,... | collective-permute-start | bytes 49160 | tf_op jit(solution)/shard_map/ppermute | solution.py:384
  105.9 1.6 %collective-permute-done.47.even_ref = bf16[1,32,256]{2,1,0:T(8,128)(2,1)S(1)} collective-permute-done((bf16[1,32,256]{2,1,0:T(8,128)(2,1)S(1)}, bf16[1,32,256]{2,1,0:T(8,128)(2,1)S(1)}, u32[]{:S(2)}, u32[]{:S(2)}) %collective-permute-start.47) | collective-permute-done | bytes 16416 | tf_op jit(solution)/shard_map/ppermute | solution.py:384
  107.5 2.1 %collective-permute-start.49 = (bf16[2,9,32,128]{3,2,1,0:T(8,128)(2,1)S(1)}, bf16[2,9,32,128]{3,2,1,0:T(8,128)(2,1)S(1)}, u32[]{:S(2)}, u32[]{:S(2)}) collective-permute-start(bf16[2,9,32,128]{3,2,1,0:T(8,128)(2,1)S(1)} %get-tuple-element.210), channel_id=1, source_target_pairs={{0,4},{1,9},{2,6},{3,11},{4,0},{5,13},{6,2},{7,15},{8,12},{9,1},{1... | collective-permute-start | bytes 442376 | tf_op jit(solution)/shard_map/ppermute | solution.py:258
  109.6 1.7 %collective-permute-start.50 = (bf16[2,9,32,128]{3,2,1,0:T(8,128)(2,1)S(1)}, bf16[2,9,32,128]{3,2,1,0:T(8,128)(2,1)S(1)}, u32[]{:S(2)}, u32[]{:S(2)}) collective-permute-start(bf16[2,9,32,128]{3,2,1,0:T(8,128)(2,1)S(1)} %get-tuple-element.211), channel_id=1, source_target_pairs={{0,8},{1,3},{2,10},{3,1},{4,12},{5,7},{6,14},{7,5},{8,0},{9,11},{1... | collective-permute-start | bytes 442376 | tf_op jit(solution)/shard_map/ppermute | solution.py:258
  111.4 2.0 %collective-permute-start.51 = (bf16[2,9,32,128]{3,2,1,0:T(8,128)(2,1)S(1)}, bf16[2,9,32,128]{3,2,1,0:T(8,128)(2,1)S(1)}, u32[]{:S(2)}, u32[]{:S(2)}) collective-permute-start(bf16[2,9,32,128]{3,2,1,0:T(8,128)(2,1)S(1)} %get-tuple-element.212), channel_id=1, source_target_pairs={{0,2},{1,5},{2,0},{3,7},{4,6},{5,1},{6,4},{7,3},{8,10},{9,13},{10,... | collective-permute-start | bytes 442376 | tf_op jit(solution)/shard_map/ppermute | solution.py:258
  113.4 1.4 %collective-permute-done.50.refs_1_ = bf16[2,9,32,128]{3,2,1,0:T(8,128)(2,1)S(1)} collective-permute-done((bf16[2,9,32,128]{3,2,1,0:T(8,128)(2,1)S(1)}, bf16[2,9,32,128]{3,2,1,0:T(8,128)(2,1)S(1)}, u32[]{:S(2)}, u32[]{:S(2)}) %collective-permute-start.50) | collective-permute-done | bytes 147488 | tf_op jit(solution)/shard_map/ppermute | solution.py:258
  114.8 4.9 %collective-permute-done.51.refs_2_ = bf16[2,9,32,128]{3,2,1,0:T(8,128)(2,1)S(1)} collective-permute-done((bf16[2,9,32,128]{3,2,1,0:T(8,128)(2,1)S(1)}, bf16[2,9,32,128]{3,2,1,0:T(8,128)(2,1)S(1)}, u32[]{:S(2)}, u32[]{:S(2)}) %collective-permute-start.51) | collective-permute-done | bytes 147488 | tf_op jit(solution)/shard_map/ppermute | solution.py:258
  119.9 1.8 %collective-permute-start.53 = (bf16[2,9,32,128]{3,2,1,0:T(8,128)(2,1)S(1)}, bf16[2,9,32,128]{3,2,1,0:T(8,128)(2,1)S(1)}, u32[]{:S(2)}, u32[]{:S(2)}) collective-permute-start(bf16[2,9,32,128]{3,2,1,0:T(8,128)(2,1)S(1)} %get-tuple-element.226), channel_id=1, source_target_pairs={{0,2},{1,5},{2,0},{3,7},{4,6},{5,1},{6,4},{7,3},{8,10},{9,13},{10,... | collective-permute-start | bytes 442376 | tf_op jit(solution)/shard_map/ppermute | solution.py:258
  121.7 1.1 collective-permute-start.54
  123.1 1.2 collective-permute-done.57.inner_ref
  124.4 1.0 collective-permute-done.58.outer_ref
  125.9 0.9 collective-permute-done.54.refs_1_
  126.8 1.1 collective-permute-done.55.refs_2_
  128.0 1.5 %collective-permute-start.59 = (bf16[9,32,128]{2,1,0:T(8,128)(2,1)S(1)}, bf16[9,32,128]{2,1,0:T(8,128)(2,1)S(1)}, u32[]{:S(2)}, u32[]{:S(2)}) collective-permute-start(bf16[9,32,128]{2,1,0:T(8,128)(2,1)S(1)} %get-tuple-element.239), channel_id=1, source_target_pairs={{0,16},{1,17},{2,18},{3,19},{4,20},{5,21},{6,22},{7,23},{8,24},{9,... | collective-permute-start | bytes 221192 | tf_op jit(solution)/shard_map/ppermute | solution.py:254
  129.5 4.3 %collective-permute-done.59.rest_0_ = bf16[9,32,128]{2,1,0:T(8,128)(2,1)S(1)} collective-permute-done((bf16[9,32,128]{2,1,0:T(8,128)(2,1)S(1)}, bf16[9,32,128]{2,1,0:T(8,128)(2,1)S(1)}, u32[]{:S(2)}, u32[]{:S(2)}) %collective-permute-start.59) | collective-permute-done | bytes 73760 | tf_op jit(solution)/shard_map/ppermute | solution.py:254
  133.9 2.5 %shard_map.114 = bf16[8,32,256]{2,1,0:T(8,128)(2,1)} custom-call(s32[12]{0:T(128)S(1)} %copy-done.7, f32[8,32,256]{2,1,0:T(8,128)S(1)} %shard_map.107.near_ref, f32[2,32,256]{2,1,0:T(8,128)S(1)} %shard_map.112.edge_ref, bf16[8,96,256]{2,1,0:T(8,128)(2,1)S(1)} %copy-done.2, bf16[8,96,96]{2,1,0:T(8,128)(2,1)S(1)} %copy-done.3, ...), custom_call_target="tpu_custom_call" | custom-call | tf_op jit(solution)/shard_map/pallas_call | solution.py:418
  (103 shorter events, 10.3 us)
Async XLA Ops:
  3.6 8.9 %collective-permute-start = (bf16[9,32,128]{2,1,0:T(8,128)(2,1)}, bf16[9,32,128]{2,1,0:T(8,128)(2,1)S(1)}, u32[]{:S(2)}, u32[]{:S(2)}) collective-permute-start(bf16[9,32,128]{2,1,0:T(8,128)(2,1)} %get-tuple-element.121.refs_0_), channel_id=1, source_target_pairs={{0,16},{1,17},{2,18},{3,19},{4,20},{5,21},{6,22},{7,23},{8,24},{9,... | collective-permute-start | bytes 221192 | tf_op jit(solution)/shard_map/ppermute | solution.py:254
  12.4 20.5 %copy-start.8 = (s32[128]{0:T(128)S(1)}, s32[128]{0:T(128)}, u32[]{:S(2)}) copy-start(s32[128]{0:T(128)} %param.14) | copy-start | bytes 1540
  12.4 20.5 %copy-start.9 = (s32[128]{0:T(128)S(1)}, s32[128]{0:T(128)}, u32[]{:S(2)}) copy-start(s32[128]{0:T(128)} %param.15) | copy-start | bytes 1540
  14.7 19.4 %copy-start.1 = (bf16[128,96,96]{2,1,0:T(8,128)(2,1)S(1)}, bf16[128,96,96]{2,1,0:T(8,128)(2,1)}, u32[]{:S(2)}) copy-start(bf16[128,96,96]{2,1,0:T(8,128)(2,1)} %copy.10._.coupling_ref) | copy-start | bytes 7077892
  14.7 6.9 %collective-permute-start.3 = (bf16[2,9,32,128]{3,2,1,0:T(8,128)(2,1)}, bf16[2,9,32,128]{3,2,1,0:T(8,128)(2,1)S(1)}, u32[]{:S(2)}, u32[]{:S(2)}) collective-permute-start(bf16[2,9,32,128]{3,2,1,0:T(8,128)(2,1)} %shard_map.96.refs_0_), channel_id=1, source_target_pairs={{0,8},{1,3},{2,10},{3,1},{4,12},{5,7},{6,14},{7,5},{8,0},{9,11},{1... | collective-permute-start | bytes 442376 | tf_op jit(solution)/shard_map/ppermute | solution.py:258
  16.3 7.2 %collective-permute-start.2 = (bf16[2,9,32,128]{3,2,1,0:T(8,128)(2,1)}, bf16[2,9,32,128]{3,2,1,0:T(8,128)(2,1)S(1)}, u32[]{:S(2)}, u32[]{:S(2)}) collective-permute-start(bf16[2,9,32,128]{3,2,1,0:T(8,128)(2,1)} %shard_map.96.refs_0_), channel_id=1, source_target_pairs={{0,4},{1,9},{2,6},{3,11},{4,0},{5,13},{6,2},{7,15},{8,12},{9,1},{1... | collective-permute-start | bytes 442376 | tf_op jit(solution)/shard_map/ppermute | solution.py:258
  17.8 8.5 %collective-permute-start.1 = (bf16[2,9,32,128]{3,2,1,0:T(8,128)(2,1)}, bf16[2,9,32,128]{3,2,1,0:T(8,128)(2,1)S(1)}, u32[]{:S(2)}, u32[]{:S(2)}) collective-permute-start(bf16[2,9,32,128]{3,2,1,0:T(8,128)(2,1)} %shard_map.96.refs_0_), channel_id=1, source_target_pairs={{0,2},{1,5},{2,0},{3,7},{4,6},{5,1},{6,4},{7,3},{8,10},{9,13},{10,... | collective-permute-start | bytes 442376 | tf_op jit(solution)/shard_map/ppermute | solution.py:258
  19.9 8.8 %collective-permute-start.7 = (bf16[2,9,32,128]{3,2,1,0:T(8,128)(2,1)S(1)}, bf16[2,9,32,128]{3,2,1,0:T(8,128)(2,1)S(1)}, u32[]{:S(2)}, u32[]{:S(2)}) collective-permute-start(bf16[2,9,32,128]{3,2,1,0:T(8,128)(2,1)S(1)} %copy-done.4), channel_id=1, source_target_pairs={{0,14},{1,15},{2,12},{3,13},{4,10},{5,11},{6,8},{7,9},{8,6},{9,7},... | collective-permute-start | bytes 442376 | tf_op jit(solution)/shard_map/ppermute | solution.py:258
  26.2 5.1 %collective-permute-start.4 = (bf16[2,9,32,128]{3,2,1,0:T(8,128)(2,1)S(1)}, bf16[2,9,32,128]{3,2,1,0:T(8,128)(2,1)S(1)}, u32[]{:S(2)}, u32[]{:S(2)}) collective-permute-start(bf16[2,9,32,128]{3,2,1,0:T(8,128)(2,1)S(1)} %collective-permute-done.1.refs_1_), channel_id=1, source_target_pairs={{0,4},{1,9},{2,6},{3,11},{4,0},{5,13},{6,2},{7,15},{8,12},{9,1},{1... | collective-permute-start | bytes 442376 | tf_op jit(solution)/shard_map/ppermute | solution.py:258
  26.2 5.1 %collective-permute-start.6 = (bf16[2,9,32,128]{3,2,1,0:T(8,128)(2,1)S(1)}, bf16[2,9,32,128]{3,2,1,0:T(8,128)(2,1)S(1)}, u32[]{:S(2)}, u32[]{:S(2)}) collective-permute-start(bf16[2,9,32,128]{3,2,1,0:T(8,128)(2,1)S(1)} %collective-permute-done.2.refs_2_), channel_id=1, source_target_pairs={{0,8},{1,3},{2,10},{3,1},{4,12},{5,7},{6,14},{7,5},{8,0},{9,11},{1... | collective-permute-start | bytes 442376 | tf_op jit(solution)/shard_map/ppermute | solution.py:258
  26.3 5.6 %collective-permute-start.5 = (bf16[2,9,32,128]{3,2,1,0:T(8,128)(2,1)S(1)}, bf16[2,9,32,128]{3,2,1,0:T(8,128)(2,1)S(1)}, u32[]{:S(2)}, u32[]{:S(2)}) collective-permute-start(bf16[2,9,32,128]{3,2,1,0:T(8,128)(2,1)S(1)} %collective-permute-done.3.refs_4_), channel_id=1, source_target_pairs={{0,2},{1,5},{2,0},{3,7},{4,6},{5,1},{6,4},{7,3},{8,10},{9,13},{10,... | collective-permute-start | bytes 442376 | tf_op jit(solution)/shard_map/ppermute | solution.py:258
  28.7 3.3 %collective-permute-start.8 = (bf16[2,9,32,128]{3,2,1,0:T(8,128)(2,1)S(1)}, bf16[2,9,32,128]{3,2,1,0:T(8,128)(2,1)S(1)}, u32[]{:S(2)}, u32[]{:S(2)}) collective-permute-start(bf16[2,9,32,128]{3,2,1,0:T(8,128)(2,1)S(1)} %copy-done.4), channel_id=1, source_target_pairs={{0,1},{1,0},{2,3},{3,2},{4,5},{5,4},{6,7},{7,6},{8,9},{9,8},{10,11... | collective-permute-start | bytes 442376 | tf_op jit(solution)/shard_map/ppermute | solution.py:263
  28.7 3.7 %collective-permute-start.9 = (bf16[2,9,32,128]{3,2,1,0:T(8,128)(2,1)S(1)}, bf16[2,9,32,128]{3,2,1,0:T(8,128)(2,1)S(1)}, u32[]{:S(2)}, u32[]{:S(2)}) collective-permute-start(bf16[2,9,32,128]{3,2,1,0:T(8,128)(2,1)S(1)} %collective-permute-done.1.refs_1_), channel_id=1, source_target_pairs={{0,1},{1,0},{2,3},{3,2},{4,5},{5,4},{6,7},{7,6},{8,9},{9,8},{10,11... | collective-permute-start | bytes 442376 | tf_op jit(solution)/shard_map/ppermute | solution.py:263
  31.4 1.4 %collective-permute-start.10 = (bf16[2,9,32,128]{3,2,1,0:T(8,128)(2,1)S(1)}, bf16[2,9,32,128]{3,2,1,0:T(8,128)(2,1)S(1)}, u32[]{:S(2)}, u32[]{:S(2)}) collective-permute-start(bf16[2,9,32,128]{3,2,1,0:T(8,128)(2,1)S(1)} %collective-permute-done.2.refs_2_), channel_id=1, source_target_pairs={{0,1},{1,0},{2,3},{3,2},{4,5},{5,4},{6,7},{7,6},{8,9},{9,8},{10,11... | collective-permute-start | bytes 442376 | tf_op jit(solution)/shard_map/ppermute | solution.py:263
  31.4 1.6 %collective-permute-start.12 = (bf16[2,9,32,128]{3,2,1,0:T(8,128)(2,1)S(1)}, bf16[2,9,32,128]{3,2,1,0:T(8,128)(2,1)S(1)}, u32[]{:S(2)}, u32[]{:S(2)}) collective-permute-start(bf16[2,9,32,128]{3,2,1,0:T(8,128)(2,1)S(1)} %collective-permute-done.3.refs_4_), channel_id=1, source_target_pairs={{0,1},{1,0},{2,3},{3,2},{4,5},{5,4},{6,7},{7,6},{8,9},{9,8},{10,11... | collective-permute-start | bytes 442376 | tf_op jit(solution)/shard_map/ppermute | solution.py:263
  31.9 1.4 %collective-permute-start.11 = (bf16[2,9,32,128]{3,2,1,0:T(8,128)(2,1)S(1)}, bf16[2,9,32,128]{3,2,1,0:T(8,128)(2,1)S(1)}, u32[]{:S(2)}, u32[]{:S(2)}) collective-permute-start(bf16[2,9,32,128]{3,2,1,0:T(8,128)(2,1)S(1)} %collective-permute-done.4.refs_3_), channel_id=1, source_target_pairs={{0,1},{1,0},{2,3},{3,2},{4,5},{5,4},{6,7},{7,6},{8,9},{9,8},{10,11... | collective-permute-start | bytes 442376 | tf_op jit(solution)/shard_map/ppermute | solution.py:263
  32.0 1.5 %collective-permute-start.13 = (bf16[2,9,32,128]{3,2,1,0:T(8,128)(2,1)S(1)}, bf16[2,9,32,128]{3,2,1,0:T(8,128)(2,1)S(1)}, u32[]{:S(2)}, u32[]{:S(2)}) collective-permute-start(bf16[2,9,32,128]{3,2,1,0:T(8,128)(2,1)S(1)} %collective-permute-done.5.refs_5_), channel_id=1, source_target_pairs={{0,1},{1,0},{2,3},{3,2},{4,5},{5,4},{6,7},{7,6},{8,9},{9,8},{10,11... | collective-permute-start | bytes 442376 | tf_op jit(solution)/shard_map/ppermute | solution.py:263
  32.4 1.4 %collective-permute-start.14 = (bf16[2,9,32,128]{3,2,1,0:T(8,128)(2,1)S(1)}, bf16[2,9,32,128]{3,2,1,0:T(8,128)(2,1)S(1)}, u32[]{:S(2)}, u32[]{:S(2)}) collective-permute-start(bf16[2,9,32,128]{3,2,1,0:T(8,128)(2,1)S(1)} %collective-permute-done.6.refs_6_), channel_id=1, source_target_pairs={{0,1},{1,0},{2,3},{3,2},{4,5},{5,4},{6,7},{7,6},{8,9},{9,8},{10,11... | collective-permute-start | bytes 442376 | tf_op jit(solution)/shard_map/ppermute | solution.py:263
  32.7 1.4 %collective-permute-start.15 = (bf16[2,9,32,128]{3,2,1,0:T(8,128)(2,1)S(1)}, bf16[2,9,32,128]{3,2,1,0:T(8,128)(2,1)S(1)}, u32[]{:S(2)}, u32[]{:S(2)}) collective-permute-start(bf16[2,9,32,128]{3,2,1,0:T(8,128)(2,1)S(1)} %collective-permute-done.7.refs_7_), channel_id=1, source_target_pairs={{0,1},{1,0},{2,3},{3,2},{4,5},{5,4},{6,7},{7,6},{8,9},{9,8},{10,11... | collective-permute-start | bytes 442376 | tf_op jit(solution)/shard_map/ppermute | solution.py:263
  34.1 26.9 %copy-start.11 = (bf16[1,32,256]{2,1,0:T(8,128)(2,1)S(1)}, bf16[1,32,256]{2,1,0:T(8,128)(2,1)}, u32[]{:S(2)}) copy-start(bf16[1,32,256]{2,1,0:T(8,128)(2,1)} %get-tuple-element.171) | copy-start | bytes 49156
  37.7 5.6 %collective-permute-start.16 = (bf16[4,2,9,32,128]{4,3,2,1,0:T(8,128)(2,1)S(1)}, bf16[4,2,9,32,128]{4,3,2,1,0:T(8,128)(2,1)S(1)}, u32[]{:S(2)}, u32[]{:S(2)}) collective-permute-start(bf16[4,2,9,32,128]{4,3,2,1,0:T(8,128)(2,1)S(1)} %get-tuple-element.144), channel_id=1, source_target_pairs={{0,1},{1,0},{2,3},{3,2},{4,5},{5,4},{6,7},{7,6},{8,9},{9,8},{10,11... | collective-permute-start | bytes 1769480 | tf_op jit(solution)/shard_map/ppermute | solution.py:263
  38.0 5.5 %collective-permute-start.18 = (bf16[1,32,256]{2,1,0:T(8,128)(2,1)S(1)}, bf16[1,32,256]{2,1,0:T(8,128)(2,1)S(1)}, u32[]{:S(2)}, u32[]{:S(2)}) collective-permute-start(bf16[1,32,256]{2,1,0:T(8,128)(2,1)S(1)} %copy-done.12), channel_id=1, source_target_pairs={{2,4},{3,5},{4,2},{5,3},{6,8},{7,9},{8,6},{9,7},{10,12},{11,13},{1... | collective-permute-start | bytes 49160 | tf_op jit(solution)/shard_map/ppermute | solution.py:384
  38.6 6.5 %collective-permute-start.17 = (bf16[1,32,256]{2,1,0:T(8,128)(2,1)S(1)}, bf16[1,32,256]{2,1,0:T(8,128)(2,1)S(1)}, u32[]{:S(2)}, u32[]{:S(2)}) collective-permute-start(bf16[1,32,256]{2,1,0:T(8,128)(2,1)S(1)} %copy-done.12), channel_id=1, source_target_pairs={{0,2},{1,3},{2,0},{3,1},{4,6},{5,7},{6,4},{7,5},{8,10},{9,11},{10,... | collective-permute-start | bytes 49160 | tf_op jit(solution)/shard_map/ppermute | solution.py:384
  45.2 12.7 %collective-permute-start.22 = (bf16[4,2,9,32,128]{4,3,2,1,0:T(8,128)(2,1)S(1)}, bf16[4,2,9,32,128]{4,3,2,1,0:T(8,128)(2,1)S(1)}, u32[]{:S(2)}, u32[]{:S(2)}) collective-permute-start(bf16[4,2,9,32,128]{4,3,2,1,0:T(8,128)(2,1)S(1)} %get-tuple-element.154), channel_id=1, source_target_pairs={{0,1},{1,0},{2,3},{3,2},{4,5},{5,4},{6,7},{7,6},{8,9},{9,8},{10,11... | collective-permute-start | bytes 1769480 | tf_op jit(solution)/shard_map/ppermute | solution.py:263
  45.2 6.5 %collective-permute-start.19 = (bf16[2,9,32,128]{3,2,1,0:T(8,128)(2,1)S(1)}, bf16[2,9,32,128]{3,2,1,0:T(8,128)(2,1)S(1)}, u32[]{:S(2)}, u32[]{:S(2)}) collective-permute-start(bf16[2,9,32,128]{3,2,1,0:T(8,128)(2,1)S(1)} %get-tuple-element.151), channel_id=1, source_target_pairs={{0,4},{1,9},{2,6},{3,11},{4,0},{5,13},{6,2},{7,15},{8,12},{9,1},{1... | collective-permute-start | bytes 442376 | tf_op jit(solution)/shard_map/ppermute | solution.py:258
  47.5 5.7 %collective-permute-start.20 = (bf16[2,9,32,128]{3,2,1,0:T(8,128)(2,1)S(1)}, bf16[2,9,32,128]{3,2,1,0:T(8,128)(2,1)S(1)}, u32[]{:S(2)}, u32[]{:S(2)}) collective-permute-start(bf16[2,9,32,128]{3,2,1,0:T(8,128)(2,1)S(1)} %get-tuple-element.152), channel_id=1, source_target_pairs={{0,8},{1,3},{2,10},{3,1},{4,12},{5,7},{6,14},{7,5},{8,0},{9,11},{1... | collective-permute-start | bytes 442376 | tf_op jit(solution)/shard_map/ppermute | solution.py:258
  49.0 8.8 %collective-permute-start.21 = (bf16[2,9,32,128]{3,2,1,0:T(8,128)(2,1)S(1)}, bf16[2,9,32,128]{3,2,1,0:T(8,128)(2,1)S(1)}, u32[]{:S(2)}, u32[]{:S(2)}) collective-permute-start(bf16[2,9,32,128]{3,2,1,0:T(8,128)(2,1)S(1)} %get-tuple-element.153), channel_id=1, source_target_pairs={{0,2},{1,5},{2,0},{3,7},{4,6},{5,1},{6,4},{7,3},{8,10},{9,13},{10,... | collective-permute-start | bytes 442376 | tf_op jit(solution)/shard_map/ppermute | solution.py:258
  51.3 12.2 %collective-permute-start.26 = (bf16[2,9,32,128]{3,2,1,0:T(8,128)(2,1)S(1)}, bf16[2,9,32,128]{3,2,1,0:T(8,128)(2,1)S(1)}, u32[]{:S(2)}, u32[]{:S(2)}) collective-permute-start(bf16[2,9,32,128]{3,2,1,0:T(8,128)(2,1)S(1)} %get-tuple-element.170), channel_id=1, source_target_pairs={{0,14},{1,15},{2,12},{3,13},{4,10},{5,11},{6,8},{7,9},{8,6},{9,7},... | collective-permute-start | bytes 442376 | tf_op jit(solution)/shard_map/ppermute | solution.py:258
  58.1 5.8 %collective-permute-start.23 = (bf16[2,9,32,128]{3,2,1,0:T(8,128)(2,1)S(1)}, bf16[2,9,32,128]{3,2,1,0:T(8,128)(2,1)S(1)}, u32[]{:S(2)}, u32[]{:S(2)}) collective-permute-start(bf16[2,9,32,128]{3,2,1,0:T(8,128)(2,1)S(1)} %get-tuple-element.167), channel_id=1, source_target_pairs={{0,2},{1,5},{2,0},{3,7},{4,6},{5,1},{6,4},{7,3},{8,10},{9,13},{10,... | collective-permute-start | bytes 442376 | tf_op jit(solution)/shard_map/ppermute | solution.py:258
  59.9 5.1 %collective-permute-start.24 = (bf16[2,9,32,128]{3,2,1,0:T(8,128)(2,1)S(1)}, bf16[2,9,32,128]{3,2,1,0:T(8,128)(2,1)S(1)}, u32[]{:S(2)}, u32[]{:S(2)}) collective-permute-start(bf16[2,9,32,128]{3,2,1,0:T(8,128)(2,1)S(1)} %get-tuple-element.168), channel_id=1, source_target_pairs={{0,4},{1,9},{2,6},{3,11},{4,0},{5,13},{6,2},{7,15},{8,12},{9,1},{1... | collective-permute-start | bytes 442376 | tf_op jit(solution)/shard_map/ppermute | solution.py:258
  60.8 5.1 %collective-permute-start.25 = (bf16[2,9,32,128]{3,2,1,0:T(8,128)(2,1)S(1)}, bf16[2,9,32,128]{3,2,1,0:T(8,128)(2,1)S(1)}, u32[]{:S(2)}, u32[]{:S(2)}) collective-permute-start(bf16[2,9,32,128]{3,2,1,0:T(8,128)(2,1)S(1)} %get-tuple-element.169), channel_id=1, source_target_pairs={{0,8},{1,3},{2,10},{3,1},{4,12},{5,7},{6,14},{7,5},{8,0},{9,11},{1... | collective-permute-start | bytes 442376 | tf_op jit(solution)/shard_map/ppermute | solution.py:258
  61.0 1.2 collective-permute-start.27
  62.2 1.2 collective-permute-start.28
  66.0 5.8 %collective-permute-start.29 = (bf16[9,32,128]{2,1,0:T(8,128)(2,1)S(1)}, bf16[9,32,128]{2,1,0:T(8,128)(2,1)S(1)}, u32[]{:S(2)}, u32[]{:S(2)}) collective-permute-start(bf16[9,32,128]{2,1,0:T(8,128)(2,1)S(1)} %get-tuple-element.180), channel_id=1, source_target_pairs={{0,16},{1,17},{2,18},{3,19},{4,20},{5,21},{6,22},{7,23},{8,24},{9,... | collective-permute-start | bytes 221192 | tf_op jit(solution)/shard_map/ppermute | solution.py:254
  74.3 5.4 %collective-permute-start.30 = (bf16[9,32,128]{2,1,0:T(8,128)(2,1)S(1)}, bf16[9,32,128]{2,1,0:T(8,128)(2,1)S(1)}, u32[]{:S(2)}, u32[]{:S(2)}) collective-permute-start(bf16[9,32,128]{2,1,0:T(8,128)(2,1)S(1)} %get-tuple-element.182.refs_0_), channel_id=1, source_target_pairs={{0,16},{1,17},{2,18},{3,19},{4,20},{5,21},{6,22},{7,23},{8,24},{9,... | collective-permute-start | bytes 221192 | tf_op jit(solution)/shard_map/ppermute | solution.py:254
  79.8 6.7 %collective-permute-start.33 = (bf16[2,9,32,128]{3,2,1,0:T(8,128)(2,1)S(1)}, bf16[2,9,32,128]{3,2,1,0:T(8,128)(2,1)S(1)}, u32[]{:S(2)}, u32[]{:S(2)}) collective-permute-start(bf16[2,9,32,128]{3,2,1,0:T(8,128)(2,1)S(1)} %shard_map.106.refs_0_), channel_id=1, source_target_pairs={{0,8},{1,3},{2,10},{3,1},{4,12},{5,7},{6,14},{7,5},{8,0},{9,11},{1... | collective-permute-start | bytes 442376 | tf_op jit(solution)/shard_map/ppermute | solution.py:258
  79.8 7.7 %collective-permute-start.32 = (bf16[2,9,32,128]{3,2,1,0:T(8,128)(2,1)S(1)}, bf16[2,9,32,128]{3,2,1,0:T(8,128)(2,1)S(1)}, u32[]{:S(2)}, u32[]{:S(2)}) collective-permute-start(bf16[2,9,32,128]{3,2,1,0:T(8,128)(2,1)S(1)} %shard_map.106.refs_0_), channel_id=1, source_target_pairs={{0,4},{1,9},{2,6},{3,11},{4,0},{5,13},{6,2},{7,15},{8,12},{9,1},{1... | collective-permute-start | bytes 442376 | tf_op jit(solution)/shard_map/ppermute | solution.py:258
  81.0 7.1 %collective-permute-start.31 = (bf16[2,9,32,128]{3,2,1,0:T(8,128)(2,1)S(1)}, bf16[2,9,32,128]{3,2,1,0:T(8,128)(2,1)S(1)}, u32[]{:S(2)}, u32[]{:S(2)}) collective-permute-start(bf16[2,9,32,128]{3,2,1,0:T(8,128)(2,1)S(1)} %shard_map.106.refs_0_), channel_id=1, source_target_pairs={{0,2},{1,5},{2,0},{3,7},{4,6},{5,1},{6,4},{7,3},{8,10},{9,13},{10,... | collective-permute-start | bytes 442376 | tf_op jit(solution)/shard_map/ppermute | solution.py:258
  83.6 7.6 %collective-permute-start.37 = (bf16[2,9,32,128]{3,2,1,0:T(8,128)(2,1)S(1)}, bf16[2,9,32,128]{3,2,1,0:T(8,128)(2,1)S(1)}, u32[]{:S(2)}, u32[]{:S(2)}) collective-permute-start(bf16[2,9,32,128]{3,2,1,0:T(8,128)(2,1)S(1)} %shard_map.106.refs_0_), channel_id=1, source_target_pairs={{0,14},{1,15},{2,12},{3,13},{4,10},{5,11},{6,8},{7,9},{8,6},{9,7},... | collective-permute-start | bytes 442376 | tf_op jit(solution)/shard_map/ppermute | solution.py:258
  88.2 5.1 %collective-permute-start.34 = (bf16[2,9,32,128]{3,2,1,0:T(8,128)(2,1)S(1)}, bf16[2,9,32,128]{3,2,1,0:T(8,128)(2,1)S(1)}, u32[]{:S(2)}, u32[]{:S(2)}) collective-permute-start(bf16[2,9,32,128]{3,2,1,0:T(8,128)(2,1)S(1)} %collective-permute-done.31.refs_1_), channel_id=1, source_target_pairs={{0,4},{1,9},{2,6},{3,11},{4,0},{5,13},{6,2},{7,15},{8,12},{9,1},{1... | collective-permute-start | bytes 442376 | tf_op jit(solution)/shard_map/ppermute | solution.py:258
  89.3 5.1 %collective-permute-start.36 = (bf16[2,9,32,128]{3,2,1,0:T(8,128)(2,1)S(1)}, bf16[2,9,32,128]{3,2,1,0:T(8,128)(2,1)S(1)}, u32[]{:S(2)}, u32[]{:S(2)}) collective-permute-start(bf16[2,9,32,128]{3,2,1,0:T(8,128)(2,1)S(1)} %collective-permute-done.32.refs_2_), channel_id=1, source_target_pairs={{0,8},{1,3},{2,10},{3,1},{4,12},{5,7},{6,14},{7,5},{8,0},{9,11},{1... | collective-permute-start | bytes 442376 | tf_op jit(solution)/shard_map/ppermute | solution.py:258
  90.1 5.1 %collective-permute-start.35 = (bf16[2,9,32,128]{3,2,1,0:T(8,128)(2,1)S(1)}, bf16[2,9,32,128]{3,2,1,0:T(8,128)(2,1)S(1)}, u32[]{:S(2)}, u32[]{:S(2)}) collective-permute-start(bf16[2,9,32,128]{3,2,1,0:T(8,128)(2,1)S(1)} %collective-permute-done.33.refs_4_), channel_id=1, source_target_pairs={{0,2},{1,5},{2,0},{3,7},{4,6},{5,1},{6,4},{7,3},{8,10},{9,13},{10,... | collective-permute-start | bytes 442376 | tf_op jit(solution)/shard_map/ppermute | solution.py:258
  91.2 4.0 %collective-permute-start.38 = (bf16[2,9,32,128]{3,2,1,0:T(8,128)(2,1)S(1)}, bf16[2,9,32,128]{3,2,1,0:T(8,128)(2,1)S(1)}, u32[]{:S(2)}, u32[]{:S(2)}) collective-permute-start(bf16[2,9,32,128]{3,2,1,0:T(8,128)(2,1)S(1)} %shard_map.106.refs_0_), channel_id=1, source_target_pairs={{0,1},{1,0},{2,3},{3,2},{4,5},{5,4},{6,7},{7,6},{8,9},{9,8},{10,11... | collective-permute-start | bytes 442376 | tf_op jit(solution)/shard_map/ppermute | solution.py:263
  91.2 4.5 %collective-permute-start.39 = (bf16[2,9,32,128]{3,2,1,0:T(8,128)(2,1)S(1)}, bf16[2,9,32,128]{3,2,1,0:T(8,128)(2,1)S(1)}, u32[]{:S(2)}, u32[]{:S(2)}) collective-permute-start(bf16[2,9,32,128]{3,2,1,0:T(8,128)(2,1)S(1)} %collective-permute-done.31.refs_1_), channel_id=1, source_target_pairs={{0,1},{1,0},{2,3},{3,2},{4,5},{5,4},{6,7},{7,6},{8,9},{9,8},{10,11... | collective-permute-start | bytes 442376 | tf_op jit(solution)/shard_map/ppermute | solution.py:263
  93.3 2.5 %collective-permute-start.40 = (bf16[2,9,32,128]{3,2,1,0:T(8,128)(2,1)S(1)}, bf16[2,9,32,128]{3,2,1,0:T(8,128)(2,1)S(1)}, u32[]{:S(2)}, u32[]{:S(2)}) collective-permute-start(bf16[2,9,32,128]{3,2,1,0:T(8,128)(2,1)S(1)} %collective-permute-done.32.refs_2_), channel_id=1, source_target_pairs={{0,1},{1,0},{2,3},{3,2},{4,5},{5,4},{6,7},{7,6},{8,9},{9,8},{10,11... | collective-permute-start | bytes 442376 | tf_op jit(solution)/shard_map/ppermute | solution.py:263
  94.4 1.9 %collective-permute-start.42 = (bf16[2,9,32,128]{3,2,1,0:T(8,128)(2,1)S(1)}, bf16[2,9,32,128]{3,2,1,0:T(8,128)(2,1)S(1)}, u32[]{:S(2)}, u32[]{:S(2)}) collective-permute-start(bf16[2,9,32,128]{3,2,1,0:T(8,128)(2,1)S(1)} %collective-permute-done.33.refs_4_), channel_id=1, source_target_pairs={{0,1},{1,0},{2,3},{3,2},{4,5},{5,4},{6,7},{7,6},{8,9},{9,8},{10,11... | collective-permute-start | bytes 442376 | tf_op jit(solution)/shard_map/ppermute | solution.py:263
  95.2 1.4 %collective-permute-start.41 = (bf16[2,9,32,128]{3,2,1,0:T(8,128)(2,1)S(1)}, bf16[2,9,32,128]{3,2,1,0:T(8,128)(2,1)S(1)}, u32[]{:S(2)}, u32[]{:S(2)}) collective-permute-start(bf16[2,9,32,128]{3,2,1,0:T(8,128)(2,1)S(1)} %collective-permute-done.34.refs_3_), channel_id=1, source_target_pairs={{0,1},{1,0},{2,3},{3,2},{4,5},{5,4},{6,7},{7,6},{8,9},{9,8},{10,11... | collective-permute-start | bytes 442376 | tf_op jit(solution)/shard_map/ppermute | solution.py:263
  95.3 1.6 %collective-permute-start.43 = (bf16[2,9,32,128]{3,2,1,0:T(8,128)(2,1)S(1)}, bf16[2,9,32,128]{3,2,1,0:T(8,128)(2,1)S(1)}, u32[]{:S(2)}, u32[]{:S(2)}) collective-permute-start(bf16[2,9,32,128]{3,2,1,0:T(8,128)(2,1)S(1)} %collective-permute-done.35.refs_5_), channel_id=1, source_target_pairs={{0,1},{1,0},{2,3},{3,2},{4,5},{5,4},{6,7},{7,6},{8,9},{9,8},{10,11... | collective-permute-start | bytes 442376 | tf_op jit(solution)/shard_map/ppermute | solution.py:263
  95.8 1.4 %collective-permute-start.44 = (bf16[2,9,32,128]{3,2,1,0:T(8,128)(2,1)S(1)}, bf16[2,9,32,128]{3,2,1,0:T(8,128)(2,1)S(1)}, u32[]{:S(2)}, u32[]{:S(2)}) collective-permute-start(bf16[2,9,32,128]{3,2,1,0:T(8,128)(2,1)S(1)} %collective-permute-done.36.refs_6_), channel_id=1, source_target_pairs={{0,1},{1,0},{2,3},{3,2},{4,5},{5,4},{6,7},{7,6},{8,9},{9,8},{10,11... | collective-permute-start | bytes 442376 | tf_op jit(solution)/shard_map/ppermute | solution.py:263
  95.8 1.5 %collective-permute-start.45 = (bf16[2,9,32,128]{3,2,1,0:T(8,128)(2,1)S(1)}, bf16[2,9,32,128]{3,2,1,0:T(8,128)(2,1)S(1)}, u32[]{:S(2)}, u32[]{:S(2)}) collective-permute-start(bf16[2,9,32,128]{3,2,1,0:T(8,128)(2,1)S(1)} %collective-permute-done.37.refs_7_), channel_id=1, source_target_pairs={{0,1},{1,0},{2,3},{3,2},{4,5},{5,4},{6,7},{7,6},{8,9},{9,8},{10,11... | collective-permute-start | bytes 442376 | tf_op jit(solution)/shard_map/ppermute | solution.py:263
  101.0 4.8 %collective-permute-start.46 = (bf16[4,2,9,32,128]{4,3,2,1,0:T(8,128)(2,1)S(1)}, bf16[4,2,9,32,128]{4,3,2,1,0:T(8,128)(2,1)S(1)}, u32[]{:S(2)}, u32[]{:S(2)}) collective-permute-start(bf16[4,2,9,32,128]{4,3,2,1,0:T(8,128)(2,1)S(1)} %get-tuple-element.203), channel_id=1, source_target_pairs={{0,1},{1,0},{2,3},{3,2},{4,5},{5,4},{6,7},{7,6},{8,9},{9,8},{10,11... | collective-permute-start | bytes 1769480 | tf_op jit(solution)/shard_map/ppermute | solution.py:263
  101.3 4.6 %collective-permute-start.48 = (bf16[1,32,256]{2,1,0:T(8,128)(2,1)S(1)}, bf16[1,32,256]{2,1,0:T(8,128)(2,1)S(1)}, u32[]{:S(2)}, u32[]{:S(2)}) collective-permute-start(bf16[1,32,256]{2,1,0:T(8,128)(2,1)S(1)} %get-tuple-element.209), channel_id=1, source_target_pairs={{2,4},{3,5},{4,2},{5,3},{6,8},{7,9},{8,6},{9,7},{10,12},{11,13},{1... | collective-permute-start | bytes 49160 | tf_op jit(solution)/shard_map/ppermute | solution.py:384
  102.0 5.6 %collective-permute-start.47 = (bf16[1,32,256]{2,1,0:T(8,128)(2,1)S(1)}, bf16[1,32,256]{2,1,0:T(8,128)(2,1)S(1)}, u32[]{:S(2)}, u32[]{:S(2)}) collective-permute-start(bf16[1,32,256]{2,1,0:T(8,128)(2,1)S(1)} %get-tuple-element.209), channel_id=1, source_target_pairs={{0,2},{1,3},{2,0},{3,1},{4,6},{5,7},{6,4},{7,5},{8,10},{9,11},{10,... | collective-permute-start | bytes 49160 | tf_op jit(solution)/shard_map/ppermute | solution.py:384
  107.5 12.1 %collective-permute-start.52 = (bf16[4,2,9,32,128]{4,3,2,1,0:T(8,128)(2,1)S(1)}, bf16[4,2,9,32,128]{4,3,2,1,0:T(8,128)(2,1)S(1)}, u32[]{:S(2)}, u32[]{:S(2)}) collective-permute-start(bf16[4,2,9,32,128]{4,3,2,1,0:T(8,128)(2,1)S(1)} %get-tuple-element.213), channel_id=1, source_target_pairs={{0,1},{1,0},{2,3},{3,2},{4,5},{5,4},{6,7},{7,6},{8,9},{9,8},{10,11... | collective-permute-start | bytes 1769480 | tf_op jit(solution)/shard_map/ppermute | solution.py:263
  107.5 5.8 %collective-permute-start.49 = (bf16[2,9,32,128]{3,2,1,0:T(8,128)(2,1)S(1)}, bf16[2,9,32,128]{3,2,1,0:T(8,128)(2,1)S(1)}, u32[]{:S(2)}, u32[]{:S(2)}) collective-permute-start(bf16[2,9,32,128]{3,2,1,0:T(8,128)(2,1)S(1)} %get-tuple-element.210), channel_id=1, source_target_pairs={{0,4},{1,9},{2,6},{3,11},{4,0},{5,13},{6,2},{7,15},{8,12},{9,1},{1... | collective-permute-start | bytes 442376 | tf_op jit(solution)/shard_map/ppermute | solution.py:258
  109.6 5.1 %collective-permute-start.50 = (bf16[2,9,32,128]{3,2,1,0:T(8,128)(2,1)S(1)}, bf16[2,9,32,128]{3,2,1,0:T(8,128)(2,1)S(1)}, u32[]{:S(2)}, u32[]{:S(2)}) collective-permute-start(bf16[2,9,32,128]{3,2,1,0:T(8,128)(2,1)S(1)} %get-tuple-element.211), channel_id=1, source_target_pairs={{0,8},{1,3},{2,10},{3,1},{4,12},{5,7},{6,14},{7,5},{8,0},{9,11},{1... | collective-permute-start | bytes 442376 | tf_op jit(solution)/shard_map/ppermute | solution.py:258
  111.4 8.3 %collective-permute-start.51 = (bf16[2,9,32,128]{3,2,1,0:T(8,128)(2,1)S(1)}, bf16[2,9,32,128]{3,2,1,0:T(8,128)(2,1)S(1)}, u32[]{:S(2)}, u32[]{:S(2)}) collective-permute-start(bf16[2,9,32,128]{3,2,1,0:T(8,128)(2,1)S(1)} %get-tuple-element.212), channel_id=1, source_target_pairs={{0,2},{1,5},{2,0},{3,7},{4,6},{5,1},{6,4},{7,3},{8,10},{9,13},{10,... | collective-permute-start | bytes 442376 | tf_op jit(solution)/shard_map/ppermute | solution.py:258
  113.4 12.2 %collective-permute-start.56 = (bf16[2,9,32,128]{3,2,1,0:T(8,128)(2,1)S(1)}, bf16[2,9,32,128]{3,2,1,0:T(8,128)(2,1)S(1)}, u32[]{:S(2)}, u32[]{:S(2)}) collective-permute-start(bf16[2,9,32,128]{3,2,1,0:T(8,128)(2,1)S(1)} %get-tuple-element.229), channel_id=1, source_target_pairs={{0,14},{1,15},{2,12},{3,13},{4,10},{5,11},{6,8},{7,9},{8,6},{9,7},... | collective-permute-start | bytes 442376 | tf_op jit(solution)/shard_map/ppermute | solution.py:258
  119.9 6.1 %collective-permute-start.53 = (bf16[2,9,32,128]{3,2,1,0:T(8,128)(2,1)S(1)}, bf16[2,9,32,128]{3,2,1,0:T(8,128)(2,1)S(1)}, u32[]{:S(2)}, u32[]{:S(2)}) collective-permute-start(bf16[2,9,32,128]{3,2,1,0:T(8,128)(2,1)S(1)} %get-tuple-element.226), channel_id=1, source_target_pairs={{0,2},{1,5},{2,0},{3,7},{4,6},{5,1},{6,4},{7,3},{8,10},{9,13},{10,... | collective-permute-start | bytes 442376 | tf_op jit(solution)/shard_map/ppermute | solution.py:258
  121.7 5.1 %collective-permute-start.54 = (bf16[2,9,32,128]{3,2,1,0:T(8,128)(2,1)S(1)}, bf16[2,9,32,128]{3,2,1,0:T(8,128)(2,1)S(1)}, u32[]{:S(2)}, u32[]{:S(2)}) collective-permute-start(bf16[2,9,32,128]{3,2,1,0:T(8,128)(2,1)S(1)} %get-tuple-element.227), channel_id=1, source_target_pairs={{0,4},{1,9},{2,6},{3,11},{4,0},{5,13},{6,2},{7,15},{8,12},{9,1},{1... | collective-permute-start | bytes 442376 | tf_op jit(solution)/shard_map/ppermute | solution.py:258
  122.8 5.1 %collective-permute-start.55 = (bf16[2,9,32,128]{3,2,1,0:T(8,128)(2,1)S(1)}, bf16[2,9,32,128]{3,2,1,0:T(8,128)(2,1)S(1)}, u32[]{:S(2)}, u32[]{:S(2)}) collective-permute-start(bf16[2,9,32,128]{3,2,1,0:T(8,128)(2,1)S(1)} %get-tuple-element.228), channel_id=1, source_target_pairs={{0,8},{1,3},{2,10},{3,1},{4,12},{5,7},{6,14},{7,5},{8,0},{9,11},{1... | collective-permute-start | bytes 442376 | tf_op jit(solution)/shard_map/ppermute | solution.py:258
  123.1 1.2 collective-permute-start.57
  124.3 1.2 collective-permute-start.58
  128.0 5.8 %collective-permute-start.59 = (bf16[9,32,128]{2,1,0:T(8,128)(2,1)S(1)}, bf16[9,32,128]{2,1,0:T(8,128)(2,1)S(1)}, u32[]{:S(2)}, u32[]{:S(2)}) collective-permute-start(bf16[9,32,128]{2,1,0:T(8,128)(2,1)S(1)} %get-tuple-element.239), channel_id=1, source_target_pairs={{0,16},{1,17},{2,18},{3,19},{4,20},{5,21},{6,22},{7,23},{8,24},{9,... | collective-permute-start | bytes 221192 | tf_op jit(solution)/shard_map/ppermute | solution.py:254
  (9 other events, 97.7 us)

commit v15 on v14

--- a/solution.py
+++ b/solution.py
@@ -48,13 +48,16 @@
     return jnp.concatenate([value, jnp.zeros((value.shape[0], LANES - value.shape[1]), value.dtype)], axis=1)
 
 
-def emit_coeffs(read_leaf, basis_ref, transfer_ref, ranks_ref, out_ref, leaves, rank_top):
+def emit_coeffs(values, basis_ref, transfer_ref, ranks_ref, out_ref, ready=None):
     mains, rhs, _ = out_ref.shape
+    leaves, rank_top, _ = basis_ref.shape
     lane = lax.broadcasted_iota(jnp.int32, (rhs, rank_top), 1)
     coeffs = []
     for i in range(leaves):
-        value = dot_t(read_leaf(i), basis_ref[i])
+        value = dot_t(values[i], basis_ref[i])
         coeffs.append(jnp.where(lane < ranks_ref[i], value, 0.0).astype(BF))
+    if ready is not None:
+        ready()
     for q in range(leaves // 2):
         value = dot(coeffs[2 * q], transfer_ref[2 * q]) + dot(coeffs[2 * q + 1], transfer_ref[2 * q + 1])
         coeffs.append(jnp.where(lane < ranks_ref[leaves + q], value, 0.0).astype(BF))
@@ -81,11 +84,13 @@
 def coeff_kernel(
     ranks_ref, v_hbm, basis_hbm, transfer_hbm, out_ref, inner_ref, outer_ref, v_ref, basis_ref, transfer_ref, sems
 ):
-    leaves, rank_top, _ = basis_ref.shape
-    for copy in fetch([(v_hbm, v_ref), (basis_hbm, basis_ref), (transfer_hbm, transfer_ref)], sems):
-        copy.wait()
+    leaves = basis_ref.shape[0]
+    copies = fetch([(v_hbm, v_ref), (basis_hbm, basis_ref), (transfer_hbm, transfer_ref)], sems)
+    copies[0].wait()
     emit_edges(v_ref, inner_ref, outer_ref)
-    emit_coeffs(lambda i: v_ref[i], basis_ref, transfer_ref, ranks_ref, out_ref, leaves, rank_top)
+    copies[1].wait()
+    values = [v_ref[i] for i in range(leaves)]
+    emit_coeffs(values, basis_ref, transfer_ref, ranks_ref, out_ref, copies[2].wait)
 
 
 def couple_kernel(source_ref, target_ref, coupling_ref, *refs, order, unroll):
@@ -161,16 +166,11 @@
 def middle_add_kernel(keep_ref, swap_ref, *refs, parts):
     part_refs, (own_out, *out_refs) = refs[:parts], refs[parts:]
     own_out[...] = keep_ref[0].astype(F32) + swap_ref[0].astype(F32)
-    for n, (part_ref, out_ref) in enumerate(zip(part_refs, out_refs)):
+    for n, out_ref in enumerate(out_refs):
         total = keep_ref[n + 1].astype(F32) + swap_ref[n + 1].astype(F32)
-        out_ref[...] = (total + part_ref[...].astype(F32)).astype(BF)
-
-
-def pick_kernel(even_ref, odd_ref, out_ref):
-    me, devices = lax.axis_index("clu"), lax.axis_size("clu")
-    row = jnp.where((me // CORES + me % CORES) % 2 == 0, even_ref[...], odd_ref[...])
-    inside = (me != CORES - 1) & (me != devices - CORES)
-    out_ref[...] = jnp.where(inside, row, jnp.zeros_like(row))
+        for part_ref in part_refs[n :: len(out_refs)]:
+            total = total + part_ref[...].astype(F32)
+        out_ref[...] = total.astype(BF)
 
 
 def rows_kernel(source_ref, target_ref, source_out, target_out, *, clusters, far, magic, shift):
@@ -217,19 +217,18 @@
     fields = [
         jnp.where(lane < ranks_ref[c], total[:, :rank_top], 0.0).astype(BF) for c, total in enumerate(sums)
     ]
-    for i in range(leaves):
-        down = fields[i].astype(F32) + dot_t(fields[leaves + i // 2], transfer_ref[i])
-        leaf_total = jnp.where(lane < ranks_ref[i], down, 0.0).astype(BF)
-        result = near_ref[i] + dot(leaf_total, basis_ref[i])
-        if i == 0:
-            result = result + edge_ref[0]
-        if i == leaves - 1:
-            result = result + edge_ref[1]
-        out_ref[i] = result.astype(BF)
+    downs = [fields[i].astype(F32) + dot_t(fields[leaves + i // 2], transfer_ref[i]) for i in range(leaves)]
+    leaf_totals = [jnp.where(lane < ranks_ref[i], down, 0.0).astype(BF) for i, down in enumerate(downs)]
+    results = [near_ref[i] + dot(leaf_total, basis_ref[i]) for i, leaf_total in enumerate(leaf_totals)]
+    results[0] = results[0] + edge_ref[0]
+    results[-1] = results[-1] + edge_ref[1]
+    results = [result.astype(BF) for result in results]
+    for i, result in enumerate(results):
+        out_ref[i] = result
     if next_refs:
         coeff_ref, inner_ref, outer_ref = next_refs
         emit_edges(out_ref, inner_ref, outer_ref)
-        emit_coeffs(lambda i: out_ref[i], basis_ref, transfer_ref, ranks_ref, coeff_ref, leaves, rank_top)
+        emit_coeffs(results, basis_ref, transfer_ref, ranks_ref, coeff_ref)
 
 
 def params(mebibytes):
@@ -355,9 +354,9 @@
         out_specs=[VMEM],
     )
     far_add = adder(add_kernel, 2, [part_shape] * 4)
-    middle_add = adder(functools.partial(middle_add_kernel, parts=3), 5, [own_shape] + [part_shape] * 3)
+    middle_add = adder(functools.partial(middle_add_kernel, parts=4), 6, [own_shape] + [part_shape] * 3)
     last_add = adder(
-        functools.partial(last_add_kernel, parts=4), 5, [shape(tile_shape, F32)] + [tile_out] * (far - 1)
+        functools.partial(last_add_kernel, parts=3), 4, [shape(tile_shape, F32)] + [tile_out] * (far - 1)
     )
 
     def finish(with_coeffs):
@@ -369,28 +368,17 @@
             compiler_params=params(16),
         )
 
-    count = devices // cores
-    halo_pairs = []
-    for parity in range(2):
-        chain = [(c, c + 1) for c in range(parity, count - 1, 2)]
-        ends = [(c, c) for c in (0, count - 1) if parity]
-        links = [link for pair in chain for link in (pair, pair[::-1])] + ends
-        halo_pairs.append([(a * cores + k, b * cores + k) for a, b in links for k in range(cores)])
-    pick = pl.pallas_call(
-        pick_kernel, out_shape=edge_shape, in_specs=[VMEM, VMEM], out_specs=VMEM, compiler_params=params(1)
-    )
-
-    def swap_halo(edge_row):
-        return [lax.ppermute(edge_row, "clu", pairs) for pairs in halo_pairs]
+    halo_pairs = [(d, d + cores) for d in range(1, devices - cores, cores)]
+    halo_pairs += [(d, d - cores) for d in range(cores, devices, cores)]
 
     def apply_matrix(field_in, coeffs, inner, outer, coupling, with_coeffs):
         away = [swap_far(coeffs, s) for s in range(1, far)]
         (column,) = first_join(coupling, coeffs, *away) if with_coeffs else join(coeffs, *away)
         got = {0: column, x: swap(column, x), y: swap(column, y), z: swap(column, z)}
-        near_sum = near(field_in, near_field)
-        got, near_sum = barrier((got, near_sum))
-        corner = swap(column, x | y | z)
+        near_sum, outer = barrier((near(field_in, near_field), outer))
+        got, near_sum, outer = barrier((got, near_sum, lax.ppermute(outer, "clu", halo_pairs)))
         other = {chip: swap_cores(part) for chip, part in got.items()}
+        corner = swap(got[x], y | z)
         got |= {x | y: swap(got[x], y), y | z: swap(got[y], z), z | x: swap(got[z], x)}
         got, corner = barrier((got, corner))
         got[x | y | z] = corner
@@ -402,18 +390,18 @@
             *[got[chip] for chip in range(chips)],
             *[other[chip] for chip in range(chips)],
         )
-        (keep_long, keep, send_long, send), outer = barrier((totals, outer))
+        keep_long, keep, send_long, send = totals
         corner, xy, yz, zx = far_add(keep_long, swap_cores(send_long))
-        corner, xy, yz, zx, send, outer = barrier((corner, xy, yz, zx, send, swap_halo(outer)))
-        to_x, to_y, to_z, swapped = barrier((swap(xy, y), swap(yz, z), swap(zx, x), swap_cores(send)))
+        corner, xy, yz, zx, send = barrier((corner, xy, yz, zx, send))
+        to_x, to_y, to_z, corner, swapped = barrier(
+            (swap(xy, y), swap(yz, z), swap(zx, x), swap(corner, y | z), swap_cores(send))
+        )
         own, to_x, to_y, to_z, inner, outer = barrier(
-            (*middle_add(keep, swapped, to_x, to_y, to_z), inner, pick(*outer))
+            (*middle_add(keep, swapped, to_x, to_y, to_z, corner), inner, outer)
         )
         edges = edge(swap_cores(inner), swap_cores(outer), near_field, near_field)
-        own, to_x, to_y, to_z, corner, edges = barrier(
-            (own, swap(to_x, x), swap(to_y, y), swap(to_z, z), swap(corner, x | y | z), edges)
-        )
-        total, *away = last_add(own, to_x, to_y, to_z, corner)
+        own, to_x, to_y, to_z, edges = barrier((own, swap(to_x, x), swap(to_y, y), swap(to_z, z), edges))
+        total, *away = last_add(own, to_x, to_y, to_z)
         terms = [swap_far(part, s + 1) for s, part in enumerate(away)]
         return finish(with_coeffs)(ranks, near_sum, edges, basis, transfer, total, *terms)
 

time: 137 us -> 128 us (0.934)
  starting transfers between devices: 54.2 us -> 47.3 us
  Pallas kernels: 19 us -> 17.2 us
    ppermute x4 -> x2, starting transfers between devices: 9.78 us -> 2.58 us  [apply_matrix(): lax.ppermute(outer, 'clu', halo_pairs)]
    ppermute x4 -> x2, waiting for transfers between devices: 3.3 us -> 8.84 us  [apply_matrix(): lax.ppermute(outer, 'clu', halo_pairs)]
    ppermute x28, starting transfers between devices: 34 us -> 30.5 us  [swap(): lax.ppermute(part, 'clu', [(d, d ^ (turned if d % cores else direction) *...]
    ppermute x4, waiting for transfers between devices: 15 us -> 11.9 us  [swap_far(): lax.ppermute(part, 'clu', [(d, (d + shift * cube) % devices) for d in ran...]
    ppermute x28, waiting for transfers between devices: 30.6 us -> 27.7 us  [swap(): lax.ppermute(part, 'clu', [(d, d ^ (turned if d % cores else direction) *...]
    ppermute x4, starting transfers between devices: 6.16 us -> 8.84 us  [swap_far(): lax.ppermute(part, 'clu', [(d, (d + shift * cube) % devices) for d in ran...]
    pallas_call x2, Pallas kernels: 4.98 us -> 3.17 us  [apply_matrix(): finish(with_coeffs)(ranks, near_sum, edges, basis, transfer, total, *terms)]
  transfers between devices with their start and end apart: 60 -> 58, of which waited for: 38 -> 39; matrix products, arithmetic and copies ran while one was open for 4% -> 4% of each run, Pallas kernels for 2% -> 1%
where the time goes in v15:
time: 128 us; the launch traced here: 127 us
  waiting for transfers between devices  55.6 us (43%)
  starting transfers between devices  47.3 us (37%)
  Pallas kernels  17.2 us (13%)
  local copies, waits for them, and re-layouts  6.34 us (5%)
    ppermute x28, starting transfers between devices, swap(): lax.ppermute(part, 'clu', [(d, d ^ (turned if d % cores else direction) *...  30.5 us
    ppermute x28, waiting for transfers between devices, swap(): lax.ppermute(part, 'clu', [(d, d ^ (turned if d % cores else direction) *...  27.7 us
    ppermute x4, waiting for transfers between devices, swap_far(): lax.ppermute(part, 'clu', [(d, (d + shift * cube) % devices) for d in ran...  11.9 us
    ppermute x2, waiting for transfers between devices, apply_matrix(): lax.ppermute(outer, 'clu', halo_pairs)  8.84 us
    ppermute x4, starting transfers between devices, swap_far(): lax.ppermute(part, 'clu', [(d, (d + shift * cube) % devices) for d in ran...  8.84 us
    pallas_call x2, Pallas kernels, apply_matrix(): couple(source_rows, target_rows, coupling, *[got[chip] for chip in range(...  7.21 us
    ppermute x24, waiting for transfers between devices, swap_cores(): return lax.ppermute(part, 'clu', [(d, d ^ 1) for d in range(devices)])  7.2 us
    unnamed x27, local copies, waits for them, and re-layouts  6.34 us
  transfers between devices with their start and end apart: 58, of which 39 were waited for; matrix products, arithmetic and copies ran while one was open for 4% of the time, Pallas kernels for 1%

profile of v15, /device:TPU:0, one launch (start us, length us, event | category | flops | bytes accessed | tf_op | source)
XLA Modules:
  0.0 127.3 jit_solution(3442453641459366218)
XLA Ops:
  0.6 2.9 %shard_map.95 = (bf16[9,32,128]{2,1,0:T(8,128)(2,1)}, bf16[1,32,256]{2,1,0:T(8,128)(2,1)}, bf16[1,32,256]{2,1,0:T(8,128)(2,1)}) custom-call(s32[12]{0:T(128)} %ranks_ref.5, bf16[8,32,256]{2,1,0:T(8,128)(2,1)} %v_ref.1, bf16[8,96,256]{2,1,0:T(8,128)(2,1)} %basis_ref.3, bf16[8,96,96]{2,1,0:T(8,128)(2,1)} %transfer_ref.3), custom_call_target="tpu_custom_call" | custom-call | tf_op jit(solution)/shard_map/pallas_call | solution.py:285
  3.6 4.1 %collective-permute-start = (bf16[9,32,128]{2,1,0:T(8,128)(2,1)}, bf16[9,32,128]{2,1,0:T(8,128)(2,1)S(1)}, u32[]{:S(2)}, u32[]{:S(2)}) collective-permute-start(bf16[9,32,128]{2,1,0:T(8,128)(2,1)} %get-tuple-element.113.refs_0_), channel_id=1, source_target_pairs={{0,16},{1,17},{2,18},{3,19},{4,20},{5,21},{6,22},{7,23},{8,24},{9,... | collective-permute-start | bytes 221192 | tf_op jit(solution)/shard_map/ppermute | solution.py:253
  7.7 4.8 %copy.10._.coupling_ref = bf16[128,96,96]{2,1,0:T(8,128)(2,1)} copy(bf16[128,96,96]{0,2,1:T(8,128)(2,1)} %param.12) | data formatting | bytes 4718592 | tf_op args[4]
  12.4 0.6 copy-done.10
  13.1 1.6 %shard_map.96.refs_0_ = bf16[2,9,32,128]{3,2,1,0:T(8,128)(2,1)} custom-call(bf16[128,96,96]{2,1,0:T(8,128)(2,1)} %copy.10._.coupling_ref, bf16[9,32,128]{2,1,0:T(8,128)(2,1)} %get-tuple-element.113.refs_0_, bf16[9,32,128]{2,1,0:T(8,128)(2,1)} %copy-done.10), custom_call_target="tpu_custom_call" | custom-call | tf_op jit(solution)/shard_map/pallas_call | solution.py:376
  14.7 1.6 %collective-permute-start.3 = (bf16[2,9,32,128]{3,2,1,0:T(8,128)(2,1)}, bf16[2,9,32,128]{3,2,1,0:T(8,128)(2,1)S(1)}, u32[]{:S(2)}, u32[]{:S(2)}) collective-permute-start(bf16[2,9,32,128]{3,2,1,0:T(8,128)(2,1)} %shard_map.96.refs_0_), channel_id=1, source_target_pairs={{0,8},{1,3},{2,10},{3,1},{4,12},{5,7},{6,14},{7,5},{8,0},{9,11},{1... | collective-permute-start | bytes 442376 | tf_op jit(solution)/shard_map/ppermute | solution.py:257
  16.2 1.5 %collective-permute-start.2 = (bf16[2,9,32,128]{3,2,1,0:T(8,128)(2,1)}, bf16[2,9,32,128]{3,2,1,0:T(8,128)(2,1)S(1)}, u32[]{:S(2)}, u32[]{:S(2)}) collective-permute-start(bf16[2,9,32,128]{3,2,1,0:T(8,128)(2,1)} %shard_map.96.refs_0_), channel_id=1, source_target_pairs={{0,4},{1,9},{2,6},{3,11},{4,0},{5,13},{6,2},{7,15},{8,12},{9,1},{1... | collective-permute-start | bytes 442376 | tf_op jit(solution)/shard_map/ppermute | solution.py:257
  17.8 1.5 %collective-permute-start.1 = (bf16[2,9,32,128]{3,2,1,0:T(8,128)(2,1)}, bf16[2,9,32,128]{3,2,1,0:T(8,128)(2,1)S(1)}, u32[]{:S(2)}, u32[]{:S(2)}) collective-permute-start(bf16[2,9,32,128]{3,2,1,0:T(8,128)(2,1)} %shard_map.96.refs_0_), channel_id=1, source_target_pairs={{0,2},{1,5},{2,0},{3,7},{4,6},{5,1},{6,4},{7,3},{8,10},{9,13},{10,... | collective-permute-start | bytes 442376 | tf_op jit(solution)/shard_map/ppermute | solution.py:257
  19.3 0.6 shard_map.97.near_ref
  19.8 1.3 %collective-permute-start.4 = (bf16[1,32,256]{2,1,0:T(8,128)(2,1)S(1)}, bf16[1,32,256]{2,1,0:T(8,128)(2,1)S(1)}, u32[]{:S(2)}, u32[]{:S(2)}) collective-permute-start(bf16[1,32,256]{2,1,0:T(8,128)(2,1)S(1)} %copy-done.12), channel_id=1, source_target_pairs={{1,3},{3,5},{5,7},{7,9},{9,11},{11,13},{13,15},{15,17},{17,19},{19... | collective-permute-start | bytes 49160 | tf_op jit(solution)/shard_map/ppermute | solution.py:379
  21.1 4.5 %collective-permute-done.4 = bf16[1,32,256]{2,1,0:T(8,128)(2,1)S(1)} collective-permute-done((bf16[1,32,256]{2,1,0:T(8,128)(2,1)S(1)}, bf16[1,32,256]{2,1,0:T(8,128)(2,1)S(1)}, u32[]{:S(2)}, u32[]{:S(2)}) %collective-permute-start.4) | collective-permute-done | bytes 16416 | tf_op jit(solution)/shard_map/ppermute | solution.py:379
  26.0 1.4 %collective-permute-start.6 = (bf16[2,9,32,128]{3,2,1,0:T(8,128)(2,1)S(1)}, bf16[2,9,32,128]{3,2,1,0:T(8,128)(2,1)S(1)}, u32[]{:S(2)}, u32[]{:S(2)}) collective-permute-start(bf16[2,9,32,128]{3,2,1,0:T(8,128)(2,1)S(1)} %collective-permute-done.3.refs_4_), channel_id=1, source_target_pairs={{0,2},{1,5},{2,0},{3,7},{4,6},{5,1},{6,4},{7,3},{8,10},{9,13},{10,... | collective-permute-start | bytes 442376 | tf_op jit(solution)/shard_map/ppermute | solution.py:257
  27.4 2.5 %collective-permute-start.8 = (bf16[2,9,32,128]{3,2,1,0:T(8,128)(2,1)S(1)}, bf16[2,9,32,128]{3,2,1,0:T(8,128)(2,1)S(1)}, u32[]{:S(2)}, u32[]{:S(2)}) collective-permute-start(bf16[2,9,32,128]{3,2,1,0:T(8,128)(2,1)S(1)} %collective-permute-done.1.refs_1_), channel_id=1, source_target_pairs={{0,12},{1,11},{2,14},{3,9},{4,8},{5,15},{6,10},{7,13},{8,4},{9,3},... | collective-permute-start | bytes 442376 | tf_op jit(solution)/shard_map/ppermute | solution.py:257
  30.0 0.5 collective-permute-start.5
  30.5 2.0 %collective-permute-done.7.refs_6_ = bf16[2,9,32,128]{3,2,1,0:T(8,128)(2,1)S(1)} collective-permute-done((bf16[2,9,32,128]{3,2,1,0:T(8,128)(2,1)S(1)}, bf16[2,9,32,128]{3,2,1,0:T(8,128)(2,1)S(1)}, u32[]{:S(2)}, u32[]{:S(2)}) %collective-permute-start.7) | collective-permute-done | bytes 147488 | tf_op jit(solution)/shard_map/ppermute | solution.py:257
  32.5 0.5 collective-permute-start.13
  33.0 1.3 collective-permute-done.8.refs_7_
  34.3 1.5 %collective-permute-done.5.refs_3_ = bf16[2,9,32,128]{3,2,1,0:T(8,128)(2,1)S(1)} collective-permute-done((bf16[2,9,32,128]{3,2,1,0:T(8,128)(2,1)S(1)}, bf16[2,9,32,128]{3,2,1,0:T(8,128)(2,1)S(1)}, u32[]{:S(2)}, u32[]{:S(2)}) %collective-permute-start.5) | collective-permute-done | bytes 147488 | tf_op jit(solution)/shard_map/ppermute | solution.py:257
  37.9 3.6 %shard_map.99 = (bf16[4,2,9,32,128]{4,3,2,1,0:T(8,128)(2,1)S(1)}, bf16[4,2,9,32,128]{4,3,2,1,0:T(8,128)(2,1)S(1)}, bf16[4,2,9,32,128]{4,3,2,1,0:T(8,128)(2,1)S(1)}, bf16[4,2,9,32,128]{4,3,2,1,0:T(8,128)(2,1)S(1)}) custom-call(s32[128]{0:T(128)S(1)} %bitcast.4, s32[128]{0:T(128)S(1)} %bitcast.6, bf16[128,96,96]{2,1,0:T(8,128)(2,1)S(1)} %copy-done.1, ...), custom_call_target="tpu_custom_call" | custom-call | flops 75497472 | bytes 10485760 | tf_op jit(solution)/shard_map/pallas_call | solution.py:386
  41.8 1.7 %collective-permute-done.17.swap_ref = bf16[4,2,9,32,128]{4,3,2,1,0:T(8,128)(2,1)S(1)} collective-permute-done((bf16[4,2,9,32,128]{4,3,2,1,0:T(8,128)(2,1)S(1)}, bf16[4,2,9,32,128]{4,3,2,1,0:T(8,128)(2,1)S(1)}, u32[]{:S(2)}, u32[]{:S(2)}) %collective-permute-start.17) | collective-permute-done | bytes 589856 | tf_op jit(solution)/shard_map/ppermute | solution.py:262
  44.1 1.4 %collective-permute-start.18 = (bf16[2,9,32,128]{3,2,1,0:T(8,128)(2,1)S(1)}, bf16[2,9,32,128]{3,2,1,0:T(8,128)(2,1)S(1)}, u32[]{:S(2)}, u32[]{:S(2)}) collective-permute-start(bf16[2,9,32,128]{3,2,1,0:T(8,128)(2,1)S(1)} %get-tuple-element.140), channel_id=1, source_target_pairs={{0,4},{1,9},{2,6},{3,11},{4,0},{5,13},{6,2},{7,15},{8,12},{9,1},{1... | collective-permute-start | bytes 442376 | tf_op jit(solution)/shard_map/ppermute | solution.py:257
  45.9 0.6 collective-permute-start.20
  46.5 1.9 %collective-permute-start.21 = (bf16[2,9,32,128]{3,2,1,0:T(8,128)(2,1)S(1)}, bf16[2,9,32,128]{3,2,1,0:T(8,128)(2,1)S(1)}, u32[]{:S(2)}, u32[]{:S(2)}) collective-permute-start(bf16[2,9,32,128]{3,2,1,0:T(8,128)(2,1)S(1)} %get-tuple-element.143), channel_id=1, source_target_pairs={{0,12},{1,11},{2,14},{3,9},{4,8},{5,15},{6,10},{7,13},{8,4},{9,3},... | collective-permute-start | bytes 442376 | tf_op jit(solution)/shard_map/ppermute | solution.py:257
  48.5 2.0 %collective-permute-done.18.refs_0_ = bf16[2,9,32,128]{3,2,1,0:T(8,128)(2,1)S(1)} collective-permute-done((bf16[2,9,32,128]{3,2,1,0:T(8,128)(2,1)S(1)}, bf16[2,9,32,128]{3,2,1,0:T(8,128)(2,1)S(1)}, u32[]{:S(2)}, u32[]{:S(2)}) %collective-permute-start.18) | collective-permute-done | bytes 147488 | tf_op jit(solution)/shard_map/ppermute | solution.py:257
  50.5 1.4 %collective-permute-done.19.refs_1_ = bf16[2,9,32,128]{3,2,1,0:T(8,128)(2,1)S(1)} collective-permute-done((bf16[2,9,32,128]{3,2,1,0:T(8,128)(2,1)S(1)}, bf16[2,9,32,128]{3,2,1,0:T(8,128)(2,1)S(1)}, u32[]{:S(2)}, u32[]{:S(2)}) %collective-permute-start.19) | collective-permute-done | bytes 147488 | tf_op jit(solution)/shard_map/ppermute | solution.py:257
  51.9 0.8 collective-permute-done.20.refs_2_
  52.7 1.3 %collective-permute-done.21.refs_3_ = bf16[2,9,32,128]{3,2,1,0:T(8,128)(2,1)S(1)} collective-permute-done((bf16[2,9,32,128]{3,2,1,0:T(8,128)(2,1)S(1)}, bf16[2,9,32,128]{3,2,1,0:T(8,128)(2,1)S(1)}, u32[]{:S(2)}, u32[]{:S(2)}) %collective-permute-start.21) | collective-permute-done | bytes 147488 | tf_op jit(solution)/shard_map/ppermute | solution.py:257
  54.3 0.8 collective-permute-start.23
  55.1 1.2 collective-permute-start.24
  57.2 0.7 collective-permute-done.26.inner_ref
  58.2 1.7 %collective-permute-done.23.refs_0_ = bf16[2,9,32,128]{3,2,1,0:T(8,128)(2,1)S(1)} collective-permute-done((bf16[2,9,32,128]{3,2,1,0:T(8,128)(2,1)S(1)}, bf16[2,9,32,128]{3,2,1,0:T(8,128)(2,1)S(1)}, u32[]{:S(2)}, u32[]{:S(2)}) %collective-permute-start.23) | collective-permute-done | bytes 147488 | tf_op jit(solution)/shard_map/ppermute | solution.py:257
  60.2 1.2 collective-permute-done.25.refs_2_
  61.5 1.9 %collective-permute-start.28 = (bf16[9,32,128]{2,1,0:T(8,128)(2,1)S(1)}, bf16[9,32,128]{2,1,0:T(8,128)(2,1)S(1)}, u32[]{:S(2)}, u32[]{:S(2)}) collective-permute-start(bf16[9,32,128]{2,1,0:T(8,128)(2,1)S(1)} %get-tuple-element.168), channel_id=1, source_target_pairs={{0,16},{1,17},{2,18},{3,19},{4,20},{5,21},{6,22},{7,23},{8,24},{9,... | collective-permute-start | bytes 221192 | tf_op jit(solution)/shard_map/ppermute | solution.py:253
  63.4 4.1 %collective-permute-done.28.rest_0_ = bf16[9,32,128]{2,1,0:T(8,128)(2,1)S(1)} collective-permute-done((bf16[9,32,128]{2,1,0:T(8,128)(2,1)S(1)}, bf16[9,32,128]{2,1,0:T(8,128)(2,1)S(1)}, u32[]{:S(2)}, u32[]{:S(2)}) %collective-permute-start.28) | collective-permute-done | bytes 73760 | tf_op jit(solution)/shard_map/ppermute | solution.py:253
  67.4 1.6 %shard_map.104 = (bf16[8,32,256]{2,1,0:T(8,128)(2,1)}, bf16[9,32,128]{2,1,0:T(8,128)(2,1)S(1)}, bf16[1,32,256]{2,1,0:T(8,128)(2,1)S(1)}, bf16[1,32,256]{2,1,0:T(8,128)(2,1)S(1)}) custom-call(s32[12]{0:T(128)S(1)} %copy-done.7, f32[8,32,256]{2,1,0:T(8,128)S(1)} %shard_map.97.near_ref, f32[2,32,256]{2,1,0:T(8,128)S(1)} %shard_map.102.edge_ref, ...), custom_call_target="tpu_custom_call" | custom-call | tf_op jit(solution)/shard_map/pallas_call | solution.py:406
  69.0 1.2 collective-permute-start.29
  70.2 4.1 %collective-permute-done.29.refs_1_ = bf16[9,32,128]{2,1,0:T(8,128)(2,1)S(1)} collective-permute-done((bf16[9,32,128]{2,1,0:T(8,128)(2,1)S(1)}, bf16[9,32,128]{2,1,0:T(8,128)(2,1)S(1)}, u32[]{:S(2)}, u32[]{:S(2)}) %collective-permute-start.29) | collective-permute-done | bytes 73760 | tf_op jit(solution)/shard_map/ppermute | solution.py:253
  74.5 1.4 %collective-permute-start.31 = (bf16[2,9,32,128]{3,2,1,0:T(8,128)(2,1)S(1)}, bf16[2,9,32,128]{3,2,1,0:T(8,128)(2,1)S(1)}, u32[]{:S(2)}, u32[]{:S(2)}) collective-permute-start(bf16[2,9,32,128]{3,2,1,0:T(8,128)(2,1)S(1)} %shard_map.105.refs_0_), channel_id=1, source_target_pairs={{0,4},{1,9},{2,6},{3,11},{4,0},{5,13},{6,2},{7,15},{8,12},{9,1},{1... | collective-permute-start | bytes 442376 | tf_op jit(solution)/shard_map/ppermute | solution.py:257
  75.9 1.4 %collective-permute-start.30 = (bf16[2,9,32,128]{3,2,1,0:T(8,128)(2,1)S(1)}, bf16[2,9,32,128]{3,2,1,0:T(8,128)(2,1)S(1)}, u32[]{:S(2)}, u32[]{:S(2)}) collective-permute-start(bf16[2,9,32,128]{3,2,1,0:T(8,128)(2,1)S(1)} %shard_map.105.refs_0_), channel_id=1, source_target_pairs={{0,2},{1,5},{2,0},{3,7},{4,6},{5,1},{6,4},{7,3},{8,10},{9,13},{10,... | collective-permute-start | bytes 442376 | tf_op jit(solution)/shard_map/ppermute | solution.py:257
  77.2 0.9 copy-done.6
  78.1 0.6 shard_map.106.near_ref
  78.7 1.3 %collective-permute-start.33 = (bf16[1,32,256]{2,1,0:T(8,128)(2,1)S(1)}, bf16[1,32,256]{2,1,0:T(8,128)(2,1)S(1)}, u32[]{:S(2)}, u32[]{:S(2)}) collective-permute-start(bf16[1,32,256]{2,1,0:T(8,128)(2,1)S(1)} %get-tuple-element.173), channel_id=1, source_target_pairs={{1,3},{3,5},{5,7},{7,9},{9,11},{11,13},{13,15},{15,17},{17,19},{19... | collective-permute-start | bytes 49160 | tf_op jit(solution)/shard_map/ppermute | solution.py:379
  80.0 4.3 %collective-permute-done.33 = bf16[1,32,256]{2,1,0:T(8,128)(2,1)S(1)} collective-permute-done((bf16[1,32,256]{2,1,0:T(8,128)(2,1)S(1)}, bf16[1,32,256]{2,1,0:T(8,128)(2,1)S(1)}, u32[]{:S(2)}, u32[]{:S(2)}) %collective-permute-start.33) | collective-permute-done | bytes 16416 | tf_op jit(solution)/shard_map/ppermute | solution.py:379
  84.4 2.2 %collective-permute-start.36 = (bf16[2,9,32,128]{3,2,1,0:T(8,128)(2,1)S(1)}, bf16[2,9,32,128]{3,2,1,0:T(8,128)(2,1)S(1)}, u32[]{:S(2)}, u32[]{:S(2)}) collective-permute-start(bf16[2,9,32,128]{3,2,1,0:T(8,128)(2,1)S(1)} %collective-permute-done.31.refs_2_), channel_id=1, source_target_pairs={{0,8},{1,3},{2,10},{3,1},{4,12},{5,7},{6,14},{7,5},{8,0},{9,11},{1... | collective-permute-start | bytes 442376 | tf_op jit(solution)/shard_map/ppermute | solution.py:257
  86.6 1.5 %collective-permute-start.35 = (bf16[2,9,32,128]{3,2,1,0:T(8,128)(2,1)S(1)}, bf16[2,9,32,128]{3,2,1,0:T(8,128)(2,1)S(1)}, u32[]{:S(2)}, u32[]{:S(2)}) collective-permute-start(bf16[2,9,32,128]{3,2,1,0:T(8,128)(2,1)S(1)} %collective-permute-done.32.refs_4_), channel_id=1, source_target_pairs={{0,2},{1,5},{2,0},{3,7},{4,6},{5,1},{6,4},{7,3},{8,10},{9,13},{10,... | collective-permute-start | bytes 442376 | tf_op jit(solution)/shard_map/ppermute | solution.py:257
  88.1 1.1 collective-permute-start.37
  90.1 1.6 %collective-permute-done.35.refs_5_ = bf16[2,9,32,128]{3,2,1,0:T(8,128)(2,1)S(1)} collective-permute-done((bf16[2,9,32,128]{3,2,1,0:T(8,128)(2,1)S(1)}, bf16[2,9,32,128]{3,2,1,0:T(8,128)(2,1)S(1)}, u32[]{:S(2)}, u32[]{:S(2)}) %collective-permute-start.35) | collective-permute-done | bytes 147488 | tf_op jit(solution)/shard_map/ppermute | solution.py:257
  91.7 2.5 %collective-permute-done.37.refs_7_ = bf16[2,9,32,128]{3,2,1,0:T(8,128)(2,1)S(1)} collective-permute-done((bf16[2,9,32,128]{3,2,1,0:T(8,128)(2,1)S(1)}, bf16[2,9,32,128]{3,2,1,0:T(8,128)(2,1)S(1)}, u32[]{:S(2)}, u32[]{:S(2)}) %collective-permute-start.37) | collective-permute-done | bytes 147488 | tf_op jit(solution)/shard_map/ppermute | solution.py:257
  94.2 1.5 %collective-permute-done.34.refs_3_ = bf16[2,9,32,128]{3,2,1,0:T(8,128)(2,1)S(1)} collective-permute-done((bf16[2,9,32,128]{3,2,1,0:T(8,128)(2,1)S(1)}, bf16[2,9,32,128]{3,2,1,0:T(8,128)(2,1)S(1)}, u32[]{:S(2)}, u32[]{:S(2)}) %collective-permute-start.34) | collective-permute-done | bytes 147488 | tf_op jit(solution)/shard_map/ppermute | solution.py:257
  97.8 3.6 %shard_map.107 = (bf16[4,2,9,32,128]{4,3,2,1,0:T(8,128)(2,1)S(1)}, bf16[4,2,9,32,128]{4,3,2,1,0:T(8,128)(2,1)S(1)}, bf16[4,2,9,32,128]{4,3,2,1,0:T(8,128)(2,1)S(1)}, bf16[4,2,9,32,128]{4,3,2,1,0:T(8,128)(2,1)S(1)}) custom-call(s32[128]{0:T(128)S(1)} %bitcast.5, s32[128]{0:T(128)S(1)} %bitcast.7, bf16[128,96,96]{2,1,0:T(8,128)(2,1)S(1)} %copy-done.1, ...), custom_call_target="tpu_custom_call" | custom-call | flops 75497472 | bytes 10485760 | tf_op jit(solution)/shard_map/pallas_call | solution.py:386
  101.8 1.7 %collective-permute-done.46.swap_ref = bf16[4,2,9,32,128]{4,3,2,1,0:T(8,128)(2,1)S(1)} collective-permute-done((bf16[4,2,9,32,128]{4,3,2,1,0:T(8,128)(2,1)S(1)}, bf16[4,2,9,32,128]{4,3,2,1,0:T(8,128)(2,1)S(1)}, u32[]{:S(2)}, u32[]{:S(2)}) %collective-permute-start.46) | collective-permute-done | bytes 589856 | tf_op jit(solution)/shard_map/ppermute | solution.py:262
  104.0 0.6 collective-permute-start.47
  104.6 1.0 collective-permute-start.48
  106.1 1.5 %collective-permute-start.50 = (bf16[2,9,32,128]{3,2,1,0:T(8,128)(2,1)S(1)}, bf16[2,9,32,128]{3,2,1,0:T(8,128)(2,1)S(1)}, u32[]{:S(2)}, u32[]{:S(2)}) collective-permute-start(bf16[2,9,32,128]{3,2,1,0:T(8,128)(2,1)S(1)} %get-tuple-element.198), channel_id=1, source_target_pairs={{0,12},{1,11},{2,14},{3,9},{4,8},{5,15},{6,10},{7,13},{8,4},{9,3},... | collective-permute-start | bytes 442376 | tf_op jit(solution)/shard_map/ppermute | solution.py:257
  107.7 2.7 %collective-permute-done.47.refs_0_ = bf16[2,9,32,128]{3,2,1,0:T(8,128)(2,1)S(1)} collective-permute-done((bf16[2,9,32,128]{3,2,1,0:T(8,128)(2,1)S(1)}, bf16[2,9,32,128]{3,2,1,0:T(8,128)(2,1)S(1)}, u32[]{:S(2)}, u32[]{:S(2)}) %collective-permute-start.47) | collective-permute-done | bytes 147488 | tf_op jit(solution)/shard_map/ppermute | solution.py:257
  110.8 1.4 %collective-permute-done.49.refs_2_ = bf16[2,9,32,128]{3,2,1,0:T(8,128)(2,1)S(1)} collective-permute-done((bf16[2,9,32,128]{3,2,1,0:T(8,128)(2,1)S(1)}, bf16[2,9,32,128]{3,2,1,0:T(8,128)(2,1)S(1)}, u32[]{:S(2)}, u32[]{:S(2)}) %collective-permute-start.49) | collective-permute-done | bytes 147488 | tf_op jit(solution)/shard_map/ppermute | solution.py:257
  112.2 1.5 %collective-permute-done.50.refs_3_ = bf16[2,9,32,128]{3,2,1,0:T(8,128)(2,1)S(1)} collective-permute-done((bf16[2,9,32,128]{3,2,1,0:T(8,128)(2,1)S(1)}, bf16[2,9,32,128]{3,2,1,0:T(8,128)(2,1)S(1)}, u32[]{:S(2)}, u32[]{:S(2)}) %collective-permute-start.50) | collective-permute-done | bytes 147488 | tf_op jit(solution)/shard_map/ppermute | solution.py:257
  114.3 0.9 collective-permute-start.53
  115.2 1.3 %collective-permute-start.54 = (bf16[2,9,32,128]{3,2,1,0:T(8,128)(2,1)S(1)}, bf16[2,9,32,128]{3,2,1,0:T(8,128)(2,1)S(1)}, u32[]{:S(2)}, u32[]{:S(2)}) collective-permute-start(bf16[2,9,32,128]{3,2,1,0:T(8,128)(2,1)S(1)} %get-tuple-element.214), channel_id=1, source_target_pairs={{0,8},{1,3},{2,10},{3,1},{4,12},{5,7},{6,14},{7,5},{8,0},{9,11},{1... | collective-permute-start | bytes 442376 | tf_op jit(solution)/shard_map/ppermute | solution.py:257
  117.0 0.7 collective-permute-done.55.inner_ref
  118.0 1.9 %collective-permute-done.52.refs_0_ = bf16[2,9,32,128]{3,2,1,0:T(8,128)(2,1)S(1)} collective-permute-done((bf16[2,9,32,128]{3,2,1,0:T(8,128)(2,1)S(1)}, bf16[2,9,32,128]{3,2,1,0:T(8,128)(2,1)S(1)}, u32[]{:S(2)}, u32[]{:S(2)}) %collective-permute-start.52) | collective-permute-done | bytes 147488 | tf_op jit(solution)/shard_map/ppermute | solution.py:257
  120.4 1.6 %collective-permute-start.57 = (bf16[9,32,128]{2,1,0:T(8,128)(2,1)S(1)}, bf16[9,32,128]{2,1,0:T(8,128)(2,1)S(1)}, u32[]{:S(2)}, u32[]{:S(2)}) collective-permute-start(bf16[9,32,128]{2,1,0:T(8,128)(2,1)S(1)} %get-tuple-element.223), channel_id=1, source_target_pairs={{0,16},{1,17},{2,18},{3,19},{4,20},{5,21},{6,22},{7,23},{8,24},{9,... | collective-permute-start | bytes 221192 | tf_op jit(solution)/shard_map/ppermute | solution.py:253
  122.0 3.7 %collective-permute-done.57.rest_0_ = bf16[9,32,128]{2,1,0:T(8,128)(2,1)S(1)} collective-permute-done((bf16[9,32,128]{2,1,0:T(8,128)(2,1)S(1)}, bf16[9,32,128]{2,1,0:T(8,128)(2,1)S(1)}, u32[]{:S(2)}, u32[]{:S(2)}) %collective-permute-start.57) | collective-permute-done | bytes 73760 | tf_op jit(solution)/shard_map/ppermute | solution.py:253
  125.7 1.6 %shard_map.112 = bf16[8,32,256]{2,1,0:T(8,128)(2,1)} custom-call(s32[12]{0:T(128)S(1)} %copy-done.7, f32[8,32,256]{2,1,0:T(8,128)S(1)} %shard_map.106.near_ref, f32[2,32,256]{2,1,0:T(8,128)S(1)} %shard_map.110.edge_ref, bf16[8,96,256]{2,1,0:T(8,128)(2,1)S(1)} %copy-done.2, bf16[8,96,96]{2,1,0:T(8,128)(2,1)S(1)} %copy-done.3, ...), custom_call_target="tpu_custom_call" | custom-call | tf_op jit(solution)/shard_map/pallas_call | solution.py:406
  (97 shorter events, 12.6 us)
Async XLA Ops:
  3.5 15.7 %copy-start = (bf16[8,3,256,256]{3,2,1,0:T(8,128)(2,1)S(1)}, bf16[8,3,256,256]{3,2,1,0:T(8,128)(2,1)}, u32[]{:S(2)}) copy-start(bf16[8,3,256,256]{3,2,1,0:T(8,128)(2,1)} %last_ref.3) | copy-start | bytes 9437188
  3.6 8.9 %collective-permute-start = (bf16[9,32,128]{2,1,0:T(8,128)(2,1)}, bf16[9,32,128]{2,1,0:T(8,128)(2,1)S(1)}, u32[]{:S(2)}, u32[]{:S(2)}) collective-permute-start(bf16[9,32,128]{2,1,0:T(8,128)(2,1)} %get-tuple-element.113.refs_0_), channel_id=1, source_target_pairs={{0,16},{1,17},{2,18},{3,19},{4,20},{5,21},{6,22},{7,23},{8,24},{9,... | collective-permute-start | bytes 221192 | tf_op jit(solution)/shard_map/ppermute | solution.py:253
  12.4 24.4 %copy-start.8 = (s32[128]{0:T(128)S(1)}, s32[128]{0:T(128)}, u32[]{:S(2)}) copy-start(s32[128]{0:T(128)} %param.14) | copy-start | bytes 1540
  12.4 24.4 %copy-start.9 = (s32[128]{0:T(128)S(1)}, s32[128]{0:T(128)}, u32[]{:S(2)}) copy-start(s32[128]{0:T(128)} %param.15) | copy-start | bytes 1540
  14.7 15.8 %copy-start.4 = (bf16[2,9,32,128]{3,2,1,0:T(8,128)(2,1)S(1)}, bf16[2,9,32,128]{3,2,1,0:T(8,128)(2,1)}, u32[]{:S(2)}) copy-start(bf16[2,9,32,128]{3,2,1,0:T(8,128)(2,1)} %shard_map.96.refs_0_) | copy-start | bytes 442372
  14.7 23.2 %copy-start.1 = (bf16[128,96,96]{2,1,0:T(8,128)(2,1)S(1)}, bf16[128,96,96]{2,1,0:T(8,128)(2,1)}, u32[]{:S(2)}) copy-start(bf16[128,96,96]{2,1,0:T(8,128)(2,1)} %copy.10._.coupling_ref) | copy-start | bytes 7077892
  14.7 11.0 %collective-permute-start.3 = (bf16[2,9,32,128]{3,2,1,0:T(8,128)(2,1)}, bf16[2,9,32,128]{3,2,1,0:T(8,128)(2,1)S(1)}, u32[]{:S(2)}, u32[]{:S(2)}) collective-permute-start(bf16[2,9,32,128]{3,2,1,0:T(8,128)(2,1)} %shard_map.96.refs_0_), channel_id=1, source_target_pairs={{0,8},{1,3},{2,10},{3,1},{4,12},{5,7},{6,14},{7,5},{8,0},{9,11},{1... | collective-permute-start | bytes 442376 | tf_op jit(solution)/shard_map/ppermute | solution.py:257
  16.2 9.4 %collective-permute-start.2 = (bf16[2,9,32,128]{3,2,1,0:T(8,128)(2,1)}, bf16[2,9,32,128]{3,2,1,0:T(8,128)(2,1)S(1)}, u32[]{:S(2)}, u32[]{:S(2)}) collective-permute-start(bf16[2,9,32,128]{3,2,1,0:T(8,128)(2,1)} %shard_map.96.refs_0_), channel_id=1, source_target_pairs={{0,4},{1,9},{2,6},{3,11},{4,0},{5,13},{6,2},{7,15},{8,12},{9,1},{1... | collective-permute-start | bytes 442376 | tf_op jit(solution)/shard_map/ppermute | solution.py:257
  17.8 7.9 %collective-permute-start.1 = (bf16[2,9,32,128]{3,2,1,0:T(8,128)(2,1)}, bf16[2,9,32,128]{3,2,1,0:T(8,128)(2,1)S(1)}, u32[]{:S(2)}, u32[]{:S(2)}) collective-permute-start(bf16[2,9,32,128]{3,2,1,0:T(8,128)(2,1)} %shard_map.96.refs_0_), channel_id=1, source_target_pairs={{0,2},{1,5},{2,0},{3,7},{4,6},{5,1},{6,4},{7,3},{8,10},{9,13},{10,... | collective-permute-start | bytes 442376 | tf_op jit(solution)/shard_map/ppermute | solution.py:257
  19.8 5.8 %collective-permute-start.4 = (bf16[1,32,256]{2,1,0:T(8,128)(2,1)S(1)}, bf16[1,32,256]{2,1,0:T(8,128)(2,1)S(1)}, u32[]{:S(2)}, u32[]{:S(2)}) collective-permute-start(bf16[1,32,256]{2,1,0:T(8,128)(2,1)S(1)} %copy-done.12), channel_id=1, source_target_pairs={{1,3},{3,5},{5,7},{7,9},{9,11},{11,13},{13,15},{15,17},{17,19},{19... | collective-permute-start | bytes 49160 | tf_op jit(solution)/shard_map/ppermute | solution.py:379
  25.7 6.8 %collective-permute-start.7 = (bf16[2,9,32,128]{3,2,1,0:T(8,128)(2,1)S(1)}, bf16[2,9,32,128]{3,2,1,0:T(8,128)(2,1)S(1)}, u32[]{:S(2)}, u32[]{:S(2)}) collective-permute-start(bf16[2,9,32,128]{3,2,1,0:T(8,128)(2,1)S(1)} %collective-permute-done.2.refs_2_), channel_id=1, source_target_pairs={{0,8},{1,3},{2,10},{3,1},{4,12},{5,7},{6,14},{7,5},{8,0},{9,11},{1... | collective-permute-start | bytes 442376 | tf_op jit(solution)/shard_map/ppermute | solution.py:257
  26.0 6.5 %collective-permute-start.6 = (bf16[2,9,32,128]{3,2,1,0:T(8,128)(2,1)S(1)}, bf16[2,9,32,128]{3,2,1,0:T(8,128)(2,1)S(1)}, u32[]{:S(2)}, u32[]{:S(2)}) collective-permute-start(bf16[2,9,32,128]{3,2,1,0:T(8,128)(2,1)S(1)} %collective-permute-done.3.refs_4_), channel_id=1, source_target_pairs={{0,2},{1,5},{2,0},{3,7},{4,6},{5,1},{6,4},{7,3},{8,10},{9,13},{10,... | collective-permute-start | bytes 442376 | tf_op jit(solution)/shard_map/ppermute | solution.py:257
  27.4 6.8 %collective-permute-start.8 = (bf16[2,9,32,128]{3,2,1,0:T(8,128)(2,1)S(1)}, bf16[2,9,32,128]{3,2,1,0:T(8,128)(2,1)S(1)}, u32[]{:S(2)}, u32[]{:S(2)}) collective-permute-start(bf16[2,9,32,128]{3,2,1,0:T(8,128)(2,1)S(1)} %collective-permute-done.1.refs_1_), channel_id=1, source_target_pairs={{0,12},{1,11},{2,14},{3,9},{4,8},{5,15},{6,10},{7,13},{8,4},{9,3},... | collective-permute-start | bytes 442376 | tf_op jit(solution)/shard_map/ppermute | solution.py:257
  30.0 5.8 %collective-permute-start.5 = (bf16[2,9,32,128]{3,2,1,0:T(8,128)(2,1)S(1)}, bf16[2,9,32,128]{3,2,1,0:T(8,128)(2,1)S(1)}, u32[]{:S(2)}, u32[]{:S(2)}) collective-permute-start(bf16[2,9,32,128]{3,2,1,0:T(8,128)(2,1)S(1)} %collective-permute-done.1.refs_1_), channel_id=1, source_target_pairs={{0,4},{1,9},{2,6},{3,11},{4,0},{5,13},{6,2},{7,15},{8,12},{9,1},{1... | collective-permute-start | bytes 442376 | tf_op jit(solution)/shard_map/ppermute | solution.py:257
  30.5 5.3 %collective-permute-start.9 = (bf16[2,9,32,128]{3,2,1,0:T(8,128)(2,1)S(1)}, bf16[2,9,32,128]{3,2,1,0:T(8,128)(2,1)S(1)}, u32[]{:S(2)}, u32[]{:S(2)}) collective-permute-start(bf16[2,9,32,128]{3,2,1,0:T(8,128)(2,1)S(1)} %copy-done.4), channel_id=1, source_target_pairs={{0,1},{1,0},{2,3},{3,2},{4,5},{5,4},{6,7},{7,6},{8,9},{9,8},{10,11... | collective-permute-start | bytes 442376 | tf_op jit(solution)/shard_map/ppermute | solution.py:262
  32.5 3.8 %collective-permute-start.11 = (bf16[2,9,32,128]{3,2,1,0:T(8,128)(2,1)S(1)}, bf16[2,9,32,128]{3,2,1,0:T(8,128)(2,1)S(1)}, u32[]{:S(2)}, u32[]{:S(2)}) collective-permute-start(bf16[2,9,32,128]{3,2,1,0:T(8,128)(2,1)S(1)} %collective-permute-done.2.refs_2_), channel_id=1, source_target_pairs={{0,1},{1,0},{2,3},{3,2},{4,5},{5,4},{6,7},{7,6},{8,9},{9,8},{10,11... | collective-permute-start | bytes 442376 | tf_op jit(solution)/shard_map/ppermute | solution.py:262
  32.5 3.9 %collective-permute-start.13 = (bf16[2,9,32,128]{3,2,1,0:T(8,128)(2,1)S(1)}, bf16[2,9,32,128]{3,2,1,0:T(8,128)(2,1)S(1)}, u32[]{:S(2)}, u32[]{:S(2)}) collective-permute-start(bf16[2,9,32,128]{3,2,1,0:T(8,128)(2,1)S(1)} %collective-permute-done.3.refs_4_), channel_id=1, source_target_pairs={{0,1},{1,0},{2,3},{3,2},{4,5},{5,4},{6,7},{7,6},{8,9},{9,8},{10,11... | collective-permute-start | bytes 442376 | tf_op jit(solution)/shard_map/ppermute | solution.py:262
  34.3 2.6 %collective-permute-start.10 = (bf16[2,9,32,128]{3,2,1,0:T(8,128)(2,1)S(1)}, bf16[2,9,32,128]{3,2,1,0:T(8,128)(2,1)S(1)}, u32[]{:S(2)}, u32[]{:S(2)}) collective-permute-start(bf16[2,9,32,128]{3,2,1,0:T(8,128)(2,1)S(1)} %collective-permute-done.1.refs_1_), channel_id=1, source_target_pairs={{0,1},{1,0},{2,3},{3,2},{4,5},{5,4},{6,7},{7,6},{8,9},{9,8},{10,11... | collective-permute-start | bytes 442376 | tf_op jit(solution)/shard_map/ppermute | solution.py:262
  35.8 1.4 %collective-permute-start.12 = (bf16[2,9,32,128]{3,2,1,0:T(8,128)(2,1)S(1)}, bf16[2,9,32,128]{3,2,1,0:T(8,128)(2,1)S(1)}, u32[]{:S(2)}, u32[]{:S(2)}) collective-permute-start(bf16[2,9,32,128]{3,2,1,0:T(8,128)(2,1)S(1)} %collective-permute-done.5.refs_3_), channel_id=1, source_target_pairs={{0,1},{1,0},{2,3},{3,2},{4,5},{5,4},{6,7},{7,6},{8,9},{9,8},{10,11... | collective-permute-start | bytes 442376 | tf_op jit(solution)/shard_map/ppermute | solution.py:262
  35.8 1.6 %collective-permute-start.14 = (bf16[2,9,32,128]{3,2,1,0:T(8,128)(2,1)S(1)}, bf16[2,9,32,128]{3,2,1,0:T(8,128)(2,1)S(1)}, u32[]{:S(2)}, u32[]{:S(2)}) collective-permute-start(bf16[2,9,32,128]{3,2,1,0:T(8,128)(2,1)S(1)} %collective-permute-done.6.refs_5_), channel_id=1, source_target_pairs={{0,1},{1,0},{2,3},{3,2},{4,5},{5,4},{6,7},{7,6},{8,9},{9,8},{10,11... | collective-permute-start | bytes 442376 | tf_op jit(solution)/shard_map/ppermute | solution.py:262
  36.3 1.4 %collective-permute-start.15 = (bf16[2,9,32,128]{3,2,1,0:T(8,128)(2,1)S(1)}, bf16[2,9,32,128]{3,2,1,0:T(8,128)(2,1)S(1)}, u32[]{:S(2)}, u32[]{:S(2)}) collective-permute-start(bf16[2,9,32,128]{3,2,1,0:T(8,128)(2,1)S(1)} %collective-permute-done.7.refs_6_), channel_id=1, source_target_pairs={{0,1},{1,0},{2,3},{3,2},{4,5},{5,4},{6,7},{7,6},{8,9},{9,8},{10,11... | collective-permute-start | bytes 442376 | tf_op jit(solution)/shard_map/ppermute | solution.py:262
  36.4 1.5 %collective-permute-start.16 = (bf16[2,9,32,128]{3,2,1,0:T(8,128)(2,1)S(1)}, bf16[2,9,32,128]{3,2,1,0:T(8,128)(2,1)S(1)}, u32[]{:S(2)}, u32[]{:S(2)}) collective-permute-start(bf16[2,9,32,128]{3,2,1,0:T(8,128)(2,1)S(1)} %collective-permute-done.8.refs_7_), channel_id=1, source_target_pairs={{0,1},{1,0},{2,3},{3,2},{4,5},{5,4},{6,7},{7,6},{8,9},{9,8},{10,11... | collective-permute-start | bytes 442376 | tf_op jit(solution)/shard_map/ppermute | solution.py:262
  37.9 18.8 %copy-start.11 = (bf16[1,32,256]{2,1,0:T(8,128)(2,1)S(1)}, bf16[1,32,256]{2,1,0:T(8,128)(2,1)}, u32[]{:S(2)}) copy-start(bf16[1,32,256]{2,1,0:T(8,128)(2,1)} %get-tuple-element.160) | copy-start | bytes 49156
  41.5 2.1 %collective-permute-start.17 = (bf16[4,2,9,32,128]{4,3,2,1,0:T(8,128)(2,1)S(1)}, bf16[4,2,9,32,128]{4,3,2,1,0:T(8,128)(2,1)S(1)}, u32[]{:S(2)}, u32[]{:S(2)}) collective-permute-start(bf16[4,2,9,32,128]{4,3,2,1,0:T(8,128)(2,1)S(1)} %get-tuple-element.134), channel_id=1, source_target_pairs={{0,1},{1,0},{2,3},{3,2},{4,5},{5,4},{6,7},{7,6},{8,9},{9,8},{10,11... | collective-permute-start | bytes 1769480 | tf_op jit(solution)/shard_map/ppermute | solution.py:262
  43.7 10.3 %collective-permute-start.22 = (bf16[4,2,9,32,128]{4,3,2,1,0:T(8,128)(2,1)S(1)}, bf16[4,2,9,32,128]{4,3,2,1,0:T(8,128)(2,1)S(1)}, u32[]{:S(2)}, u32[]{:S(2)}) collective-permute-start(bf16[4,2,9,32,128]{4,3,2,1,0:T(8,128)(2,1)S(1)} %get-tuple-element.144), channel_id=1, source_target_pairs={{0,1},{1,0},{2,3},{3,2},{4,5},{5,4},{6,7},{7,6},{8,9},{9,8},{10,11... | collective-permute-start | bytes 1769480 | tf_op jit(solution)/shard_map/ppermute | solution.py:262
  44.1 6.5 %collective-permute-start.18 = (bf16[2,9,32,128]{3,2,1,0:T(8,128)(2,1)S(1)}, bf16[2,9,32,128]{3,2,1,0:T(8,128)(2,1)S(1)}, u32[]{:S(2)}, u32[]{:S(2)}) collective-permute-start(bf16[2,9,32,128]{3,2,1,0:T(8,128)(2,1)S(1)} %get-tuple-element.140), channel_id=1, source_target_pairs={{0,4},{1,9},{2,6},{3,11},{4,0},{5,13},{6,2},{7,15},{8,12},{9,1},{1... | collective-permute-start | bytes 442376 | tf_op jit(solution)/shard_map/ppermute | solution.py:257
  45.4 6.4 %collective-permute-start.19 = (bf16[2,9,32,128]{3,2,1,0:T(8,128)(2,1)S(1)}, bf16[2,9,32,128]{3,2,1,0:T(8,128)(2,1)S(1)}, u32[]{:S(2)}, u32[]{:S(2)}) collective-permute-start(bf16[2,9,32,128]{3,2,1,0:T(8,128)(2,1)S(1)} %get-tuple-element.141), channel_id=1, source_target_pairs={{0,8},{1,3},{2,10},{3,1},{4,12},{5,7},{6,14},{7,5},{8,0},{9,11},{1... | collective-permute-start | bytes 442376 | tf_op jit(solution)/shard_map/ppermute | solution.py:257
  45.9 6.7 %collective-permute-start.20 = (bf16[2,9,32,128]{3,2,1,0:T(8,128)(2,1)S(1)}, bf16[2,9,32,128]{3,2,1,0:T(8,128)(2,1)S(1)}, u32[]{:S(2)}, u32[]{:S(2)}) collective-permute-start(bf16[2,9,32,128]{3,2,1,0:T(8,128)(2,1)S(1)} %get-tuple-element.142), channel_id=1, source_target_pairs={{0,2},{1,5},{2,0},{3,7},{4,6},{5,1},{6,4},{7,3},{8,10},{9,13},{10,... | collective-permute-start | bytes 442376 | tf_op jit(solution)/shard_map/ppermute | solution.py:257
  46.5 7.5 %collective-permute-start.21 = (bf16[2,9,32,128]{3,2,1,0:T(8,128)(2,1)S(1)}, bf16[2,9,32,128]{3,2,1,0:T(8,128)(2,1)S(1)}, u32[]{:S(2)}, u32[]{:S(2)}) collective-permute-start(bf16[2,9,32,128]{3,2,1,0:T(8,128)(2,1)S(1)} %get-tuple-element.143), channel_id=1, source_target_pairs={{0,12},{1,11},{2,14},{3,9},{4,8},{5,15},{6,10},{7,13},{8,4},{9,3},... | collective-permute-start | bytes 442376 | tf_op jit(solution)/shard_map/ppermute | solution.py:257
  54.3 5.6 %collective-permute-start.23 = (bf16[2,9,32,128]{3,2,1,0:T(8,128)(2,1)S(1)}, bf16[2,9,32,128]{3,2,1,0:T(8,128)(2,1)S(1)}, u32[]{:S(2)}, u32[]{:S(2)}) collective-permute-start(bf16[2,9,32,128]{3,2,1,0:T(8,128)(2,1)S(1)} %get-tuple-element.157), channel_id=1, source_target_pairs={{0,2},{1,5},{2,0},{3,7},{4,6},{5,1},{6,4},{7,3},{8,10},{9,13},{10,... | collective-permute-start | bytes 442376 | tf_op jit(solution)/shard_map/ppermute | solution.py:257
  55.1 5.1 %collective-permute-start.24 = (bf16[2,9,32,128]{3,2,1,0:T(8,128)(2,1)S(1)}, bf16[2,9,32,128]{3,2,1,0:T(8,128)(2,1)S(1)}, u32[]{:S(2)}, u32[]{:S(2)}) collective-permute-start(bf16[2,9,32,128]{3,2,1,0:T(8,128)(2,1)S(1)} %get-tuple-element.158), channel_id=1, source_target_pairs={{0,4},{1,9},{2,6},{3,11},{4,0},{5,13},{6,2},{7,15},{8,12},{9,1},{1... | collective-permute-start | bytes 442376 | tf_op jit(solution)/shard_map/ppermute | solution.py:257
  56.2 5.1 %collective-permute-start.25 = (bf16[2,9,32,128]{3,2,1,0:T(8,128)(2,1)S(1)}, bf16[2,9,32,128]{3,2,1,0:T(8,128)(2,1)S(1)}, u32[]{:S(2)}, u32[]{:S(2)}) collective-permute-start(bf16[2,9,32,128]{3,2,1,0:T(8,128)(2,1)S(1)} %get-tuple-element.159), channel_id=1, source_target_pairs={{0,8},{1,3},{2,10},{3,1},{4,12},{5,7},{6,14},{7,5},{8,0},{9,11},{1... | collective-permute-start | bytes 442376 | tf_op jit(solution)/shard_map/ppermute | solution.py:257
  56.7 1.2 collective-permute-start.26
  56.7 1.3 %collective-permute-start.27 = (bf16[1,32,256]{2,1,0:T(8,128)(2,1)S(1)}, bf16[1,32,256]{2,1,0:T(8,128)(2,1)S(1)}, u32[]{:S(2)}, u32[]{:S(2)}) collective-permute-start(bf16[1,32,256]{2,1,0:T(8,128)(2,1)S(1)} %collective-permute-done.4), channel_id=1, source_target_pairs={{0,1},{1,0},{2,3},{3,2},{4,5},{5,4},{6,7},{7,6},{8,9},{9,8},{10,11... | collective-permute-start | bytes 49160 | tf_op jit(solution)/shard_map/ppermute | solution.py:262
  61.5 6.0 %collective-permute-start.28 = (bf16[9,32,128]{2,1,0:T(8,128)(2,1)S(1)}, bf16[9,32,128]{2,1,0:T(8,128)(2,1)S(1)}, u32[]{:S(2)}, u32[]{:S(2)}) collective-permute-start(bf16[9,32,128]{2,1,0:T(8,128)(2,1)S(1)} %get-tuple-element.168), channel_id=1, source_target_pairs={{0,16},{1,17},{2,18},{3,19},{4,20},{5,21},{6,22},{7,23},{8,24},{9,... | collective-permute-start | bytes 221192 | tf_op jit(solution)/shard_map/ppermute | solution.py:253
  69.0 5.3 %collective-permute-start.29 = (bf16[9,32,128]{2,1,0:T(8,128)(2,1)S(1)}, bf16[9,32,128]{2,1,0:T(8,128)(2,1)S(1)}, u32[]{:S(2)}, u32[]{:S(2)}) collective-permute-start(bf16[9,32,128]{2,1,0:T(8,128)(2,1)S(1)} %get-tuple-element.170.refs_0_), channel_id=1, source_target_pairs={{0,16},{1,17},{2,18},{3,19},{4,20},{5,21},{6,22},{7,23},{8,24},{9,... | collective-permute-start | bytes 221192 | tf_op jit(solution)/shard_map/ppermute | solution.py:253
  74.4 10.0 %collective-permute-start.32 = (bf16[2,9,32,128]{3,2,1,0:T(8,128)(2,1)S(1)}, bf16[2,9,32,128]{3,2,1,0:T(8,128)(2,1)S(1)}, u32[]{:S(2)}, u32[]{:S(2)}) collective-permute-start(bf16[2,9,32,128]{3,2,1,0:T(8,128)(2,1)S(1)} %shard_map.105.refs_0_), channel_id=1, source_target_pairs={{0,8},{1,3},{2,10},{3,1},{4,12},{5,7},{6,14},{7,5},{8,0},{9,11},{1... | collective-permute-start | bytes 442376 | tf_op jit(solution)/shard_map/ppermute | solution.py:257
  74.5 9.9 %collective-permute-start.31 = (bf16[2,9,32,128]{3,2,1,0:T(8,128)(2,1)S(1)}, bf16[2,9,32,128]{3,2,1,0:T(8,128)(2,1)S(1)}, u32[]{:S(2)}, u32[]{:S(2)}) collective-permute-start(bf16[2,9,32,128]{3,2,1,0:T(8,128)(2,1)S(1)} %shard_map.105.refs_0_), channel_id=1, source_target_pairs={{0,4},{1,9},{2,6},{3,11},{4,0},{5,13},{6,2},{7,15},{8,12},{9,1},{1... | collective-permute-start | bytes 442376 | tf_op jit(solution)/shard_map/ppermute | solution.py:257
  75.9 8.5 %collective-permute-start.30 = (bf16[2,9,32,128]{3,2,1,0:T(8,128)(2,1)S(1)}, bf16[2,9,32,128]{3,2,1,0:T(8,128)(2,1)S(1)}, u32[]{:S(2)}, u32[]{:S(2)}) collective-permute-start(bf16[2,9,32,128]{3,2,1,0:T(8,128)(2,1)S(1)} %shard_map.105.refs_0_), channel_id=1, source_target_pairs={{0,2},{1,5},{2,0},{3,7},{4,6},{5,1},{6,4},{7,3},{8,10},{9,13},{10,... | collective-permute-start | bytes 442376 | tf_op jit(solution)/shard_map/ppermute | solution.py:257
  78.7 5.6 %collective-permute-start.33 = (bf16[1,32,256]{2,1,0:T(8,128)(2,1)S(1)}, bf16[1,32,256]{2,1,0:T(8,128)(2,1)S(1)}, u32[]{:S(2)}, u32[]{:S(2)}) collective-permute-start(bf16[1,32,256]{2,1,0:T(8,128)(2,1)S(1)} %get-tuple-element.173), channel_id=1, source_target_pairs={{1,3},{3,5},{5,7},{7,9},{9,11},{11,13},{13,15},{15,17},{17,19},{19... | collective-permute-start | bytes 49160 | tf_op jit(solution)/shard_map/ppermute | solution.py:379
  84.4 5.4 %collective-permute-start.36 = (bf16[2,9,32,128]{3,2,1,0:T(8,128)(2,1)S(1)}, bf16[2,9,32,128]{3,2,1,0:T(8,128)(2,1)S(1)}, u32[]{:S(2)}, u32[]{:S(2)}) collective-permute-start(bf16[2,9,32,128]{3,2,1,0:T(8,128)(2,1)S(1)} %collective-permute-done.31.refs_2_), channel_id=1, source_target_pairs={{0,8},{1,3},{2,10},{3,1},{4,12},{5,7},{6,14},{7,5},{8,0},{9,11},{1... | collective-permute-start | bytes 442376 | tf_op jit(solution)/shard_map/ppermute | solution.py:257
  86.6 5.1 %collective-permute-start.35 = (bf16[2,9,32,128]{3,2,1,0:T(8,128)(2,1)S(1)}, bf16[2,9,32,128]{3,2,1,0:T(8,128)(2,1)S(1)}, u32[]{:S(2)}, u32[]{:S(2)}) collective-permute-start(bf16[2,9,32,128]{3,2,1,0:T(8,128)(2,1)S(1)} %collective-permute-done.32.refs_4_), channel_id=1, source_target_pairs={{0,2},{1,5},{2,0},{3,7},{4,6},{5,1},{6,4},{7,3},{8,10},{9,13},{10,... | collective-permute-start | bytes 442376 | tf_op jit(solution)/shard_map/ppermute | solution.py:257
  88.1 6.1 %collective-permute-start.37 = (bf16[2,9,32,128]{3,2,1,0:T(8,128)(2,1)S(1)}, bf16[2,9,32,128]{3,2,1,0:T(8,128)(2,1)S(1)}, u32[]{:S(2)}, u32[]{:S(2)}) collective-permute-start(bf16[2,9,32,128]{3,2,1,0:T(8,128)(2,1)S(1)} %collective-permute-done.30.refs_1_), channel_id=1, source_target_pairs={{0,12},{1,11},{2,14},{3,9},{4,8},{5,15},{6,10},{7,13},{8,4},{9,3},... | collective-permute-start | bytes 442376 | tf_op jit(solution)/shard_map/ppermute | solution.py:257
  89.1 6.5 %collective-permute-start.34 = (bf16[2,9,32,128]{3,2,1,0:T(8,128)(2,1)S(1)}, bf16[2,9,32,128]{3,2,1,0:T(8,128)(2,1)S(1)}, u32[]{:S(2)}, u32[]{:S(2)}) collective-permute-start(bf16[2,9,32,128]{3,2,1,0:T(8,128)(2,1)S(1)} %collective-permute-done.30.refs_1_), channel_id=1, source_target_pairs={{0,4},{1,9},{2,6},{3,11},{4,0},{5,13},{6,2},{7,15},{8,12},{9,1},{1... | collective-permute-start | bytes 442376 | tf_op jit(solution)/shard_map/ppermute | solution.py:257
  89.6 6.1 %collective-permute-start.38 = (bf16[2,9,32,128]{3,2,1,0:T(8,128)(2,1)S(1)}, bf16[2,9,32,128]{3,2,1,0:T(8,128)(2,1)S(1)}, u32[]{:S(2)}, u32[]{:S(2)}) collective-permute-start(bf16[2,9,32,128]{3,2,1,0:T(8,128)(2,1)S(1)} %shard_map.105.refs_0_), channel_id=1, source_target_pairs={{0,1},{1,0},{2,3},{3,2},{4,5},{5,4},{6,7},{7,6},{8,9},{9,8},{10,11... | collective-permute-start | bytes 442376 | tf_op jit(solution)/shard_map/ppermute | solution.py:262
  89.8 6.4 %collective-permute-start.40 = (bf16[2,9,32,128]{3,2,1,0:T(8,128)(2,1)S(1)}, bf16[2,9,32,128]{3,2,1,0:T(8,128)(2,1)S(1)}, u32[]{:S(2)}, u32[]{:S(2)}) collective-permute-start(bf16[2,9,32,128]{3,2,1,0:T(8,128)(2,1)S(1)} %collective-permute-done.31.refs_2_), channel_id=1, source_target_pairs={{0,1},{1,0},{2,3},{3,2},{4,5},{5,4},{6,7},{7,6},{8,9},{9,8},{10,11... | collective-permute-start | bytes 442376 | tf_op jit(solution)/shard_map/ppermute | solution.py:262
  91.7 4.6 %collective-permute-start.42 = (bf16[2,9,32,128]{3,2,1,0:T(8,128)(2,1)S(1)}, bf16[2,9,32,128]{3,2,1,0:T(8,128)(2,1)S(1)}, u32[]{:S(2)}, u32[]{:S(2)}) collective-permute-start(bf16[2,9,32,128]{3,2,1,0:T(8,128)(2,1)S(1)} %collective-permute-done.32.refs_4_), channel_id=1, source_target_pairs={{0,1},{1,0},{2,3},{3,2},{4,5},{5,4},{6,7},{7,6},{8,9},{9,8},{10,11... | collective-permute-start | bytes 442376 | tf_op jit(solution)/shard_map/ppermute | solution.py:262
  94.2 2.5 %collective-permute-start.39 = (bf16[2,9,32,128]{3,2,1,0:T(8,128)(2,1)S(1)}, bf16[2,9,32,128]{3,2,1,0:T(8,128)(2,1)S(1)}, u32[]{:S(2)}, u32[]{:S(2)}) collective-permute-start(bf16[2,9,32,128]{3,2,1,0:T(8,128)(2,1)S(1)} %collective-permute-done.30.refs_1_), channel_id=1, source_target_pairs={{0,1},{1,0},{2,3},{3,2},{4,5},{5,4},{6,7},{7,6},{8,9},{9,8},{10,11... | collective-permute-start | bytes 442376 | tf_op jit(solution)/shard_map/ppermute | solution.py:262
  95.7 1.4 %collective-permute-start.41 = (bf16[2,9,32,128]{3,2,1,0:T(8,128)(2,1)S(1)}, bf16[2,9,32,128]{3,2,1,0:T(8,128)(2,1)S(1)}, u32[]{:S(2)}, u32[]{:S(2)}) collective-permute-start(bf16[2,9,32,128]{3,2,1,0:T(8,128)(2,1)S(1)} %collective-permute-done.34.refs_3_), channel_id=1, source_target_pairs={{0,1},{1,0},{2,3},{3,2},{4,5},{5,4},{6,7},{7,6},{8,9},{9,8},{10,11... | collective-permute-start | bytes 442376 | tf_op jit(solution)/shard_map/ppermute | solution.py:262
  95.7 1.6 %collective-permute-start.43 = (bf16[2,9,32,128]{3,2,1,0:T(8,128)(2,1)S(1)}, bf16[2,9,32,128]{3,2,1,0:T(8,128)(2,1)S(1)}, u32[]{:S(2)}, u32[]{:S(2)}) collective-permute-start(bf16[2,9,32,128]{3,2,1,0:T(8,128)(2,1)S(1)} %collective-permute-done.35.refs_5_), channel_id=1, source_target_pairs={{0,1},{1,0},{2,3},{3,2},{4,5},{5,4},{6,7},{7,6},{8,9},{9,8},{10,11... | collective-permute-start | bytes 442376 | tf_op jit(solution)/shard_map/ppermute | solution.py:262
  96.2 1.4 %collective-permute-start.44 = (bf16[2,9,32,128]{3,2,1,0:T(8,128)(2,1)S(1)}, bf16[2,9,32,128]{3,2,1,0:T(8,128)(2,1)S(1)}, u32[]{:S(2)}, u32[]{:S(2)}) collective-permute-start(bf16[2,9,32,128]{3,2,1,0:T(8,128)(2,1)S(1)} %collective-permute-done.36.refs_6_), channel_id=1, source_target_pairs={{0,1},{1,0},{2,3},{3,2},{4,5},{5,4},{6,7},{7,6},{8,9},{9,8},{10,11... | collective-permute-start | bytes 442376 | tf_op jit(solution)/shard_map/ppermute | solution.py:262
  96.3 1.5 %collective-permute-start.45 = (bf16[2,9,32,128]{3,2,1,0:T(8,128)(2,1)S(1)}, bf16[2,9,32,128]{3,2,1,0:T(8,128)(2,1)S(1)}, u32[]{:S(2)}, u32[]{:S(2)}) collective-permute-start(bf16[2,9,32,128]{3,2,1,0:T(8,128)(2,1)S(1)} %collective-permute-done.37.refs_7_), channel_id=1, source_target_pairs={{0,1},{1,0},{2,3},{3,2},{4,5},{5,4},{6,7},{7,6},{8,9},{9,8},{10,11... | collective-permute-start | bytes 442376 | tf_op jit(solution)/shard_map/ppermute | solution.py:262
  101.4 2.1 %collective-permute-start.46 = (bf16[4,2,9,32,128]{4,3,2,1,0:T(8,128)(2,1)S(1)}, bf16[4,2,9,32,128]{4,3,2,1,0:T(8,128)(2,1)S(1)}, u32[]{:S(2)}, u32[]{:S(2)}) collective-permute-start(bf16[4,2,9,32,128]{4,3,2,1,0:T(8,128)(2,1)S(1)} %get-tuple-element.189), channel_id=1, source_target_pairs={{0,1},{1,0},{2,3},{3,2},{4,5},{5,4},{6,7},{7,6},{8,9},{9,8},{10,11... | collective-permute-start | bytes 1769480 | tf_op jit(solution)/shard_map/ppermute | solution.py:262
  103.6 10.1 %collective-permute-start.51 = (bf16[4,2,9,32,128]{4,3,2,1,0:T(8,128)(2,1)S(1)}, bf16[4,2,9,32,128]{4,3,2,1,0:T(8,128)(2,1)S(1)}, u32[]{:S(2)}, u32[]{:S(2)}) collective-permute-start(bf16[4,2,9,32,128]{4,3,2,1,0:T(8,128)(2,1)S(1)} %get-tuple-element.199), channel_id=1, source_target_pairs={{0,1},{1,0},{2,3},{3,2},{4,5},{5,4},{6,7},{7,6},{8,9},{9,8},{10,11... | collective-permute-start | bytes 1769480 | tf_op jit(solution)/shard_map/ppermute | solution.py:262
  104.0 6.4 %collective-permute-start.47 = (bf16[2,9,32,128]{3,2,1,0:T(8,128)(2,1)S(1)}, bf16[2,9,32,128]{3,2,1,0:T(8,128)(2,1)S(1)}, u32[]{:S(2)}, u32[]{:S(2)}) collective-permute-start(bf16[2,9,32,128]{3,2,1,0:T(8,128)(2,1)S(1)} %get-tuple-element.195), channel_id=1, source_target_pairs={{0,4},{1,9},{2,6},{3,11},{4,0},{5,13},{6,2},{7,15},{8,12},{9,1},{1... | collective-permute-start | bytes 442376 | tf_op jit(solution)/shard_map/ppermute | solution.py:257
  104.6 6.2 %collective-permute-start.48 = (bf16[2,9,32,128]{3,2,1,0:T(8,128)(2,1)S(1)}, bf16[2,9,32,128]{3,2,1,0:T(8,128)(2,1)S(1)}, u32[]{:S(2)}, u32[]{:S(2)}) collective-permute-start(bf16[2,9,32,128]{3,2,1,0:T(8,128)(2,1)S(1)} %get-tuple-element.196), channel_id=1, source_target_pairs={{0,8},{1,3},{2,10},{3,1},{4,12},{5,7},{6,14},{7,5},{8,0},{9,11},{1... | collective-permute-start | bytes 442376 | tf_op jit(solution)/shard_map/ppermute | solution.py:257
  105.6 6.6 %collective-permute-start.49 = (bf16[2,9,32,128]{3,2,1,0:T(8,128)(2,1)S(1)}, bf16[2,9,32,128]{3,2,1,0:T(8,128)(2,1)S(1)}, u32[]{:S(2)}, u32[]{:S(2)}) collective-permute-start(bf16[2,9,32,128]{3,2,1,0:T(8,128)(2,1)S(1)} %get-tuple-element.197), channel_id=1, source_target_pairs={{0,2},{1,5},{2,0},{3,7},{4,6},{5,1},{6,4},{7,3},{8,10},{9,13},{10,... | collective-permute-start | bytes 442376 | tf_op jit(solution)/shard_map/ppermute | solution.py:257
  106.1 7.6 %collective-permute-start.50 = (bf16[2,9,32,128]{3,2,1,0:T(8,128)(2,1)S(1)}, bf16[2,9,32,128]{3,2,1,0:T(8,128)(2,1)S(1)}, u32[]{:S(2)}, u32[]{:S(2)}) collective-permute-start(bf16[2,9,32,128]{3,2,1,0:T(8,128)(2,1)S(1)} %get-tuple-element.198), channel_id=1, source_target_pairs={{0,12},{1,11},{2,14},{3,9},{4,8},{5,15},{6,10},{7,13},{8,4},{9,3},... | collective-permute-start | bytes 442376 | tf_op jit(solution)/shard_map/ppermute | solution.py:257
  114.0 5.9 %collective-permute-start.52 = (bf16[2,9,32,128]{3,2,1,0:T(8,128)(2,1)S(1)}, bf16[2,9,32,128]{3,2,1,0:T(8,128)(2,1)S(1)}, u32[]{:S(2)}, u32[]{:S(2)}) collective-permute-start(bf16[2,9,32,128]{3,2,1,0:T(8,128)(2,1)S(1)} %get-tuple-element.212), channel_id=1, source_target_pairs={{0,2},{1,5},{2,0},{3,7},{4,6},{5,1},{6,4},{7,3},{8,10},{9,13},{10,... | collective-permute-start | bytes 442376 | tf_op jit(solution)/shard_map/ppermute | solution.py:257
  114.3 5.6 %collective-permute-start.53 = (bf16[2,9,32,128]{3,2,1,0:T(8,128)(2,1)S(1)}, bf16[2,9,32,128]{3,2,1,0:T(8,128)(2,1)S(1)}, u32[]{:S(2)}, u32[]{:S(2)}) collective-permute-start(bf16[2,9,32,128]{3,2,1,0:T(8,128)(2,1)S(1)} %get-tuple-element.213), channel_id=1, source_target_pairs={{0,4},{1,9},{2,6},{3,11},{4,0},{5,13},{6,2},{7,15},{8,12},{9,1},{1... | collective-permute-start | bytes 442376 | tf_op jit(solution)/shard_map/ppermute | solution.py:257
  115.2 5.1 %collective-permute-start.54 = (bf16[2,9,32,128]{3,2,1,0:T(8,128)(2,1)S(1)}, bf16[2,9,32,128]{3,2,1,0:T(8,128)(2,1)S(1)}, u32[]{:S(2)}, u32[]{:S(2)}) collective-permute-start(bf16[2,9,32,128]{3,2,1,0:T(8,128)(2,1)S(1)} %get-tuple-element.214), channel_id=1, source_target_pairs={{0,8},{1,3},{2,10},{3,1},{4,12},{5,7},{6,14},{7,5},{8,0},{9,11},{1... | collective-permute-start | bytes 442376 | tf_op jit(solution)/shard_map/ppermute | solution.py:257
  116.5 1.2 collective-permute-start.55
  116.5 1.3 %collective-permute-start.56 = (bf16[1,32,256]{2,1,0:T(8,128)(2,1)S(1)}, bf16[1,32,256]{2,1,0:T(8,128)(2,1)S(1)}, u32[]{:S(2)}, u32[]{:S(2)}) collective-permute-start(bf16[1,32,256]{2,1,0:T(8,128)(2,1)S(1)} %collective-permute-done.33), channel_id=1, source_target_pairs={{0,1},{1,0},{2,3},{3,2},{4,5},{5,4},{6,7},{7,6},{8,9},{9,8},{10,11... | collective-permute-start | bytes 49160 | tf_op jit(solution)/shard_map/ppermute | solution.py:262
  120.4 5.3 %collective-permute-start.57 = (bf16[9,32,128]{2,1,0:T(8,128)(2,1)S(1)}, bf16[9,32,128]{2,1,0:T(8,128)(2,1)S(1)}, u32[]{:S(2)}, u32[]{:S(2)}) collective-permute-start(bf16[9,32,128]{2,1,0:T(8,128)(2,1)S(1)} %get-tuple-element.223), channel_id=1, source_target_pairs={{0,16},{1,17},{2,18},{3,19},{4,20},{5,21},{6,22},{7,23},{8,24},{9,... | collective-permute-start | bytes 221192 | tf_op jit(solution)/shard_map/ppermute | solution.py:253
  (7 other events, 64.3 us)

commit v16 on v15

--- a/solution.py
+++ b/solution.py
@@ -95,9 +95,14 @@
 
 def couple_kernel(source_ref, target_ref, coupling_ref, *refs, order, unroll):
     chips = sum(len(group) for group in order)
-    in_refs, out_refs, (sources, total) = refs[: 2 * chips], refs[2 * chips : -2], refs[-2:]
     blocks, rank_top, _ = coupling_ref.shape
-    far, mains, rhs, _ = in_refs[0].shape
+    near_size, far, mains, rhs, _ = refs[0].shape
+    per_core = 1 + chips - near_size
+    in_refs, out_refs, (sources, total) = [], refs[2 * per_core : -2], refs[-2:]
+    for core in range(2):
+        joined, *single = refs[core * per_core : (core + 1) * per_core]
+        pieces = {chip: joined.at[place] for place, chip in enumerate(order[1])} | dict(zip(order[0], single))
+        in_refs += [pieces[chip] for chip in range(chips)]
     quads = mains // 3
     clusters = mains + quads
 
@@ -138,6 +143,10 @@
         return 0
 
     lax.fori_loop(0, far, pack, 0)
+
+
+def order_kernel(_, __, out_ref):
+    out_ref[...] = jnp.zeros_like(out_ref)
 
 
 def near_kernel(v_ref, near_ref, out_ref):
@@ -299,7 +308,7 @@
     couple = pl.pallas_call(
         functools.partial(couple_kernel, order=order, unroll=64),
         out_shape=[shape((4, far) + tile_shape, BF)] * 4,
-        in_specs=[SMEM, SMEM, VMEM] + [VMEM] * (cores * chips),
+        in_specs=[SMEM, SMEM, VMEM] + [VMEM] * (cores * (1 + len(order[0]))),
         out_specs=[VMEM] * 4,
         scratch_shapes=[
             pltpu.VMEM((devices * clusters, rhs, LANES), BF),
@@ -347,11 +356,19 @@
 
     own_shape = shape((far,) + tile_shape, F32)
     join = adder(join_kernel, far, [part_shape])
+    join_near = adder(join_kernel, 4, [shape((4,) + part_shape.shape, BF)])
+    relaid = pl.pallas_call(
+        order_kernel,
+        out_shape=shape((8, LANES), F32),
+        in_specs=[pl.BlockSpec(memory_space=pl.ANY)] * 2,
+        out_specs=VMEM,
+    )
     first_join = pl.pallas_call(
         lambda _, *refs: join_kernel(*refs),
         out_shape=[part_shape],
         in_specs=[pl.BlockSpec(memory_space=pl.ANY)] + [VMEM] * far,
         out_specs=[VMEM],
+        compiler_params=params(16),
     )
     far_add = adder(add_kernel, 2, [part_shape] * 4)
     middle_add = adder(functools.partial(middle_add_kernel, parts=4), 6, [own_shape] + [part_shape] * 3)
@@ -373,23 +390,17 @@
 
     def apply_matrix(field_in, coeffs, inner, outer, coupling, with_coeffs):
         away = [swap_far(coeffs, s) for s in range(1, far)]
-        (column,) = first_join(coupling, coeffs, *away) if with_coeffs else join(coeffs, *away)
+        (column,) = first_join(relaid(coupling, coeffs), coeffs, *away) if with_coeffs else join(coeffs, *away)
         got = {0: column, x: swap(column, x), y: swap(column, y), z: swap(column, z)}
-        near_sum, outer = barrier((near(field_in, near_field), outer))
-        got, near_sum, outer = barrier((got, near_sum, lax.ppermute(outer, "clu", halo_pairs)))
-        other = {chip: swap_cores(part) for chip, part in got.items()}
+        near_sum = near(field_in, near_field)
+        got, near_sum = barrier((got, near_sum))
         corner = swap(got[x], y | z)
+        (near_pieces,) = join_near(*[got[chip] for chip in order[1]])
         got |= {x | y: swap(got[x], y), y | z: swap(got[y], z), z | x: swap(got[z], x)}
-        got, corner = barrier((got, corner))
         got[x | y | z] = corner
-        other |= {chip: swap_cores(got[chip]) for chip in order[0]}
-        totals = couple(
-            source_rows,
-            target_rows,
-            coupling,
-            *[got[chip] for chip in range(chips)],
-            *[other[chip] for chip in range(chips)],
-        )
+        far_pieces, other_near = barrier(([got[chip] for chip in order[0]], swap_cores(near_pieces)))
+        other_far = [swap_cores(part) for part in far_pieces]
+        totals = couple(source_rows, target_rows, coupling, near_pieces, *far_pieces, other_near, *other_far)
         keep_long, keep, send_long, send = totals
         corner, xy, yz, zx = far_add(keep_long, swap_cores(send_long))
         corner, xy, yz, zx, send = barrier((corner, xy, yz, zx, send))
@@ -399,10 +410,12 @@
         own, to_x, to_y, to_z, inner, outer = barrier(
             (*middle_add(keep, swapped, to_x, to_y, to_z, corner), inner, outer)
         )
+        own, to_x, to_y, to_z, inner, outer = barrier(
+            (own, swap(to_x, x), swap(to_y, y), swap(to_z, z), inner, lax.ppermute(outer, "clu", halo_pairs))
+        )
+        total, *away = last_add(own, to_x, to_y, to_z)
         edges = edge(swap_cores(inner), swap_cores(outer), near_field, near_field)
-        own, to_x, to_y, to_z, edges = barrier((own, swap(to_x, x), swap(to_y, y), swap(to_z, z), edges))
-        total, *away = last_add(own, to_x, to_y, to_z)
-        terms = [swap_far(part, s + 1) for s, part in enumerate(away)]
+        terms, edges = barrier(([swap_far(part, s + 1) for s, part in enumerate(away)], edges))
         return finish(with_coeffs)(ranks, near_sum, edges, basis, transfer, total, *terms)
 
     first, *second_args = apply_matrix(charges, first_coeffs, inner, outer, coupling, True)

time: 128 us -> 127 us (level)
    ppermute x28, starting transfers between devices: 30.5 us -> 34.5 us  [swap(): lax.ppermute(part, 'clu', [(d, d ^ (turned if d % cores else direction) *...]
    ppermute x4, starting transfers between devices: 8.84 us -> 6.26 us  [swap_far(): lax.ppermute(part, 'clu', [(d, (d + shift * cube) % devices) for d in ran...]
    ppermute x28, waiting for transfers between devices: 27.7 us -> 26.4 us  [swap(): lax.ppermute(part, 'clu', [(d, d ^ (turned if d % cores else direction) *...]
    pallas_call x5 -> x8, Pallas kernels: 9.99 us -> 9.08 us  [the longest x2 7.21 us: apply_matrix(): couple(source_rows, target_rows, coupling, near_pieces, *far_pieces, othe...]
    ppermute x24 -> x18, starting transfers between devices: 5.35 us -> 4.49 us  [swap_cores(): return lax.ppermute(part, 'clu', [(d, d ^ 1) for d in range(devices)])]
    ppermute x24 -> x18, waiting for transfers between devices: 7.2 us -> 7.58 us  [swap_cores(): return lax.ppermute(part, 'clu', [(d, d ^ 1) for d in range(devices)])]
  transfers between devices with their start and end apart: 58 -> 52, of which waited for: 39 -> 37; matrix products, arithmetic and copies ran while one was open for 4% -> 4% of each run, Pallas kernels for 1% -> 2%
where the time goes in v16:
time: 127 us
  waiting for transfers between devices  55.5 us (44%)
  starting transfers between devices  47.8 us (38%)
  Pallas kernels  16.3 us (13%)
  local copies, waits for them, and re-layouts  6.55 us (5%)
    ppermute x28, starting transfers between devices, swap(): lax.ppermute(part, 'clu', [(d, d ^ (turned if d % cores else direction) *...  34.5 us
    ppermute x28, waiting for transfers between devices, swap(): lax.ppermute(part, 'clu', [(d, d ^ (turned if d % cores else direction) *...  26.4 us
    ppermute x4, waiting for transfers between devices, swap_far(): lax.ppermute(part, 'clu', [(d, (d + shift * cube) % devices) for d in ran...  12.8 us
    ppermute x2, waiting for transfers between devices, apply_matrix(): lax.ppermute(outer, 'clu', halo_pairs)  8.67 us
    ppermute x18, waiting for transfers between devices, swap_cores(): return lax.ppermute(part, 'clu', [(d, d ^ 1) for d in range(devices)])  7.58 us
    pallas_call x2, Pallas kernels, apply_matrix(): couple(source_rows, target_rows, coupling, near_pieces, *far_pieces, othe...  7.21 us
    unnamed x27, local copies, waits for them, and re-layouts  6.55 us
    ppermute x4, starting transfers between devices, swap_far(): lax.ppermute(part, 'clu', [(d, (d + shift * cube) % devices) for d in ran...  6.26 us
  transfers between devices with their start and end apart: 52, of which 37 were waited for; matrix products, arithmetic and copies ran while one was open for 4% of the time, Pallas kernels for 2%

profile of v16, /device:TPU:0, one launch (start us, length us, event | category | flops | bytes accessed | tf_op | source)
XLA Modules:
  0.0 127.0 jit_solution(14366921061976092545)
XLA Ops:
  0.6 2.9 %shard_map.95 = (bf16[9,32,128]{2,1,0:T(8,128)(2,1)}, bf16[1,32,256]{2,1,0:T(8,128)(2,1)}, bf16[1,32,256]{2,1,0:T(8,128)(2,1)}) custom-call(s32[12]{0:T(128)} %ranks_ref.5, bf16[8,32,256]{2,1,0:T(8,128)(2,1)} %v_ref.1, bf16[8,96,256]{2,1,0:T(8,128)(2,1)} %basis_ref.3, bf16[8,96,96]{2,1,0:T(8,128)(2,1)} %transfer_ref.3), custom_call_target="tpu_custom_call" | custom-call | tf_op jit(solution)/shard_map/pallas_call | solution.py:294
  3.6 4.1 %collective-permute-start = (bf16[9,32,128]{2,1,0:T(8,128)(2,1)}, bf16[9,32,128]{2,1,0:T(8,128)(2,1)S(1)}, u32[]{:S(2)}, u32[]{:S(2)}) collective-permute-start(bf16[9,32,128]{2,1,0:T(8,128)(2,1)} %get-tuple-element.107.__.refs_0_), channel_id=1, source_target_pairs={{0,16},{1,17},{2,18},{3,19},{4,20},{5,21},{6,22},{7,23},{8,24},{9,... | collective-permute-start | bytes 221192 | tf_op jit(solution)/shard_map/ppermute | solution.py:262
  7.7 4.8 %copy.10._.coupling_ref = bf16[128,96,96]{2,1,0:T(8,128)(2,1)} copy(bf16[128,96,96]{0,2,1:T(8,128)(2,1)} %param.12) | data formatting | bytes 4718592 | tf_op args[4]
  12.4 0.6 shard_map.96._
  13.0 0.8 copy-done.7
  13.9 1.6 %collective-permute-start.3 = (bf16[2,9,32,128]{3,2,1,0:T(8,128)(2,1)S(1)}, bf16[2,9,32,128]{3,2,1,0:T(8,128)(2,1)S(1)}, u32[]{:S(2)}, u32[]{:S(2)}) collective-permute-start(bf16[2,9,32,128]{3,2,1,0:T(8,128)(2,1)S(1)} %shard_map.97.refs_0_), channel_id=1, source_target_pairs={{0,8},{1,3},{2,10},{3,1},{4,12},{5,7},{6,14},{7,5},{8,0},{9,11},{1... | collective-permute-start | bytes 442376 | tf_op jit(solution)/shard_map/ppermute | solution.py:266
  15.5 1.5 %collective-permute-start.2 = (bf16[2,9,32,128]{3,2,1,0:T(8,128)(2,1)S(1)}, bf16[2,9,32,128]{3,2,1,0:T(8,128)(2,1)S(1)}, u32[]{:S(2)}, u32[]{:S(2)}) collective-permute-start(bf16[2,9,32,128]{3,2,1,0:T(8,128)(2,1)S(1)} %shard_map.97.refs_0_), channel_id=1, source_target_pairs={{0,4},{1,9},{2,6},{3,11},{4,0},{5,13},{6,2},{7,15},{8,12},{9,1},{1... | collective-permute-start | bytes 442376 | tf_op jit(solution)/shard_map/ppermute | solution.py:266
  17.0 1.5 %collective-permute-start.1 = (bf16[2,9,32,128]{3,2,1,0:T(8,128)(2,1)S(1)}, bf16[2,9,32,128]{3,2,1,0:T(8,128)(2,1)S(1)}, u32[]{:S(2)}, u32[]{:S(2)}) collective-permute-start(bf16[2,9,32,128]{3,2,1,0:T(8,128)(2,1)S(1)} %shard_map.97.refs_0_), channel_id=1, source_target_pairs={{0,2},{1,5},{2,0},{3,7},{4,6},{5,1},{6,4},{7,3},{8,10},{9,13},{10,... | collective-permute-start | bytes 442376 | tf_op jit(solution)/shard_map/ppermute | solution.py:266
  18.5 0.6 shard_map.98.near_ref
  19.1 1.3 %collective-permute-done.3.refs_3_ = bf16[2,9,32,128]{3,2,1,0:T(8,128)(2,1)S(1)} collective-permute-done((bf16[2,9,32,128]{3,2,1,0:T(8,128)(2,1)S(1)}, bf16[2,9,32,128]{3,2,1,0:T(8,128)(2,1)S(1)}, u32[]{:S(2)}, u32[]{:S(2)}) %collective-permute-start.3) | collective-permute-done | bytes 147488 | tf_op jit(solution)/shard_map/ppermute | solution.py:266
  20.5 1.3 %collective-permute-done.2.refs_2_ = bf16[2,9,32,128]{3,2,1,0:T(8,128)(2,1)S(1)} collective-permute-done((bf16[2,9,32,128]{3,2,1,0:T(8,128)(2,1)S(1)}, bf16[2,9,32,128]{3,2,1,0:T(8,128)(2,1)S(1)}, u32[]{:S(2)}, u32[]{:S(2)}) %collective-permute-start.2) | collective-permute-done | bytes 147488 | tf_op jit(solution)/shard_map/ppermute | solution.py:266
  22.3 0.5 collective-permute-start.6
  22.8 1.5 %collective-permute-start.7 = (bf16[2,9,32,128]{3,2,1,0:T(8,128)(2,1)S(1)}, bf16[2,9,32,128]{3,2,1,0:T(8,128)(2,1)S(1)}, u32[]{:S(2)}, u32[]{:S(2)}) collective-permute-start(bf16[2,9,32,128]{3,2,1,0:T(8,128)(2,1)S(1)} %collective-permute-done.3.refs_3_), channel_id=1, source_target_pairs={{0,2},{1,5},{2,0},{3,7},{4,6},{5,1},{6,4},{7,3},{8,10},{9,13},{10,... | collective-permute-start | bytes 442376 | tf_op jit(solution)/shard_map/ppermute | solution.py:266
  24.8 2.5 %collective-permute-start.4 = (bf16[2,9,32,128]{3,2,1,0:T(8,128)(2,1)S(1)}, bf16[2,9,32,128]{3,2,1,0:T(8,128)(2,1)S(1)}, u32[]{:S(2)}, u32[]{:S(2)}) collective-permute-start(bf16[2,9,32,128]{3,2,1,0:T(8,128)(2,1)S(1)} %collective-permute-done.1.refs_1_), channel_id=1, source_target_pairs={{0,12},{1,11},{2,14},{3,9},{4,8},{5,15},{6,10},{7,13},{8,4},{9,3},... | collective-permute-start | bytes 442376 | tf_op jit(solution)/shard_map/ppermute | solution.py:266
  27.4 0.9 collective-permute-done.6.refs_3_
  28.6 1.6 %collective-permute-done.5.refs_2_ = bf16[2,9,32,128]{3,2,1,0:T(8,128)(2,1)S(1)} collective-permute-done((bf16[2,9,32,128]{3,2,1,0:T(8,128)(2,1)S(1)}, bf16[2,9,32,128]{3,2,1,0:T(8,128)(2,1)S(1)}, u32[]{:S(2)}, u32[]{:S(2)}) %collective-permute-start.5) | collective-permute-done | bytes 147488 | tf_op jit(solution)/shard_map/ppermute | solution.py:266
  30.2 2.3 %collective-permute-done.4.refs_1_ = bf16[2,9,32,128]{3,2,1,0:T(8,128)(2,1)S(1)} collective-permute-done((bf16[2,9,32,128]{3,2,1,0:T(8,128)(2,1)S(1)}, bf16[2,9,32,128]{3,2,1,0:T(8,128)(2,1)S(1)}, u32[]{:S(2)}, u32[]{:S(2)}) %collective-permute-start.4) | collective-permute-done | bytes 147488 | tf_op jit(solution)/shard_map/ppermute | solution.py:266
  34.9 3.6 %shard_map.101 = (bf16[4,2,9,32,128]{4,3,2,1,0:T(8,128)(2,1)S(1)}, bf16[4,2,9,32,128]{4,3,2,1,0:T(8,128)(2,1)S(1)}, bf16[4,2,9,32,128]{4,3,2,1,0:T(8,128)(2,1)S(1)}, bf16[4,2,9,32,128]{4,3,2,1,0:T(8,128)(2,1)S(1)}) custom-call(s32[128]{0:T(128)S(1)} %bitcast.4, s32[128]{0:T(128)S(1)} %bitcast.6, bf16[128,96,96]{2,1,0:T(8,128)(2,1)S(1)} %copy-done.1, ...), custom_call_target="tpu_custom_call" | custom-call | flops 75497472 | bytes 10485760 | tf_op jit(solution)/shard_map/pallas_call | solution.py:403
  38.8 1.8 %collective-permute-done.13.swap_ref = bf16[4,2,9,32,128]{4,3,2,1,0:T(8,128)(2,1)S(1)} collective-permute-done((bf16[4,2,9,32,128]{4,3,2,1,0:T(8,128)(2,1)S(1)}, bf16[4,2,9,32,128]{4,3,2,1,0:T(8,128)(2,1)S(1)}, u32[]{:S(2)}, u32[]{:S(2)}) %collective-permute-start.13) | collective-permute-done | bytes 589856 | tf_op jit(solution)/shard_map/ppermute | solution.py:271
  41.0 1.0 collective-permute-start.14
  42.5 1.5 %collective-permute-start.16 = (bf16[2,9,32,128]{3,2,1,0:T(8,128)(2,1)S(1)}, bf16[2,9,32,128]{3,2,1,0:T(8,128)(2,1)S(1)}, u32[]{:S(2)}, u32[]{:S(2)}) collective-permute-start(bf16[2,9,32,128]{3,2,1,0:T(8,128)(2,1)S(1)} %get-tuple-element.130), channel_id=1, source_target_pairs={{0,2},{1,5},{2,0},{3,7},{4,6},{5,1},{6,4},{7,3},{8,10},{9,13},{10,... | collective-permute-start | bytes 442376 | tf_op jit(solution)/shard_map/ppermute | solution.py:266
  44.0 1.5 %collective-permute-start.17 = (bf16[2,9,32,128]{3,2,1,0:T(8,128)(2,1)S(1)}, bf16[2,9,32,128]{3,2,1,0:T(8,128)(2,1)S(1)}, u32[]{:S(2)}, u32[]{:S(2)}) collective-permute-start(bf16[2,9,32,128]{3,2,1,0:T(8,128)(2,1)S(1)} %get-tuple-element.131), channel_id=1, source_target_pairs={{0,12},{1,11},{2,14},{3,9},{4,8},{5,15},{6,10},{7,13},{8,4},{9,3},... | collective-permute-start | bytes 442376 | tf_op jit(solution)/shard_map/ppermute | solution.py:266
  45.4 2.2 %collective-permute-done.14.refs_0_ = bf16[2,9,32,128]{3,2,1,0:T(8,128)(2,1)S(1)} collective-permute-done((bf16[2,9,32,128]{3,2,1,0:T(8,128)(2,1)S(1)}, bf16[2,9,32,128]{3,2,1,0:T(8,128)(2,1)S(1)}, u32[]{:S(2)}, u32[]{:S(2)}) %collective-permute-start.14) | collective-permute-done | bytes 147488 | tf_op jit(solution)/shard_map/ppermute | solution.py:266
  47.6 0.8 collective-permute-done.15.refs_1_
  48.4 2.3 %collective-permute-done.17.refs_3_ = bf16[2,9,32,128]{3,2,1,0:T(8,128)(2,1)S(1)} collective-permute-done((bf16[2,9,32,128]{3,2,1,0:T(8,128)(2,1)S(1)}, bf16[2,9,32,128]{3,2,1,0:T(8,128)(2,1)S(1)}, u32[]{:S(2)}, u32[]{:S(2)}) %collective-permute-start.17) | collective-permute-done | bytes 147488 | tf_op jit(solution)/shard_map/ppermute | solution.py:266
  51.0 1.0 collective-permute-start.19
  52.0 1.1 collective-permute-start.20
  53.1 0.9 collective-permute-start.21
  54.0 1.3 %collective-permute-start.22 = (bf16[1,32,256]{2,1,0:T(8,128)(2,1)S(1)}, bf16[1,32,256]{2,1,0:T(8,128)(2,1)S(1)}, u32[]{:S(2)}, u32[]{:S(2)}) collective-permute-start(bf16[1,32,256]{2,1,0:T(8,128)(2,1)S(1)} %copy-done.12), channel_id=1, source_target_pairs={{1,3},{3,5},{5,7},{7,9},{9,11},{11,13},{13,15},{15,17},{17,19},{19... | collective-permute-start | bytes 49160 | tf_op jit(solution)/shard_map/ppermute | solution.py:414
  55.3 4.3 %collective-permute-done.22 = bf16[1,32,256]{2,1,0:T(8,128)(2,1)S(1)} collective-permute-done((bf16[1,32,256]{2,1,0:T(8,128)(2,1)S(1)}, bf16[1,32,256]{2,1,0:T(8,128)(2,1)S(1)}, u32[]{:S(2)}, u32[]{:S(2)}) %collective-permute-start.22) | collective-permute-done | bytes 16416 | tf_op jit(solution)/shard_map/ppermute | solution.py:414
  59.8 1.2 collective-permute-start.23
  61.5 0.7 collective-permute-done.24.inner_ref
  62.5 3.4 %collective-permute-done.23.rest_0_ = bf16[9,32,128]{2,1,0:T(8,128)(2,1)S(1)} collective-permute-done((bf16[9,32,128]{2,1,0:T(8,128)(2,1)S(1)}, bf16[9,32,128]{2,1,0:T(8,128)(2,1)S(1)}, u32[]{:S(2)}, u32[]{:S(2)}) %collective-permute-start.23) | collective-permute-done | bytes 73760 | tf_op jit(solution)/shard_map/ppermute | solution.py:262
  65.9 1.6 %shard_map.106 = (bf16[8,32,256]{2,1,0:T(8,128)(2,1)}, bf16[9,32,128]{2,1,0:T(8,128)(2,1)S(1)}, bf16[1,32,256]{2,1,0:T(8,128)(2,1)S(1)}, bf16[1,32,256]{2,1,0:T(8,128)(2,1)S(1)}) custom-call(s32[12]{0:T(128)S(1)} %copy-done.8, f32[8,32,256]{2,1,0:T(8,128)S(1)} %shard_map.98.near_ref, f32[2,32,256]{2,1,0:T(8,128)S(1)} %shard_map.105.edge_ref, ...), custom_call_target="tpu_custom_call" | custom-call | tf_op jit(solution)/shard_map/pallas_call | solution.py:419
  67.9 5.5 %collective-permute-done.26.refs_1_ = bf16[9,32,128]{2,1,0:T(8,128)(2,1)S(1)} collective-permute-done((bf16[9,32,128]{2,1,0:T(8,128)(2,1)S(1)}, bf16[9,32,128]{2,1,0:T(8,128)(2,1)S(1)}, u32[]{:S(2)}, u32[]{:S(2)}) %collective-permute-start.26) | collective-permute-done | bytes 73760 | tf_op jit(solution)/shard_map/ppermute | solution.py:262
  73.6 0.9 collective-permute-start.28
  74.4 3.0 %collective-permute-start.27 = (bf16[2,9,32,128]{3,2,1,0:T(8,128)(2,1)S(1)}, bf16[2,9,32,128]{3,2,1,0:T(8,128)(2,1)S(1)}, u32[]{:S(2)}, u32[]{:S(2)}) collective-permute-start(bf16[2,9,32,128]{3,2,1,0:T(8,128)(2,1)S(1)} %shard_map.107.refs_0_), channel_id=1, source_target_pairs={{0,2},{1,5},{2,0},{3,7},{4,6},{5,1},{6,4},{7,3},{8,10},{9,13},{10,... | collective-permute-start | bytes 442376 | tf_op jit(solution)/shard_map/ppermute | solution.py:266
  77.4 0.9 copy-done.6
  78.3 0.6 shard_map.108.near_ref
  79.0 1.6 %collective-permute-done.27.refs_1_ = bf16[2,9,32,128]{3,2,1,0:T(8,128)(2,1)S(1)} collective-permute-done((bf16[2,9,32,128]{3,2,1,0:T(8,128)(2,1)S(1)}, bf16[2,9,32,128]{3,2,1,0:T(8,128)(2,1)S(1)}, u32[]{:S(2)}, u32[]{:S(2)}) %collective-permute-start.27) | collective-permute-done | bytes 147488 | tf_op jit(solution)/shard_map/ppermute | solution.py:266
  80.7 2.0 %collective-permute-start.32 = (bf16[2,9,32,128]{3,2,1,0:T(8,128)(2,1)S(1)}, bf16[2,9,32,128]{3,2,1,0:T(8,128)(2,1)S(1)}, u32[]{:S(2)}, u32[]{:S(2)}) collective-permute-start(bf16[2,9,32,128]{3,2,1,0:T(8,128)(2,1)S(1)} %collective-permute-done.28.refs_2_), channel_id=1, source_target_pairs={{0,8},{1,3},{2,10},{3,1},{4,12},{5,7},{6,14},{7,5},{8,0},{9,11},{1... | collective-permute-start | bytes 442376 | tf_op jit(solution)/shard_map/ppermute | solution.py:266
  82.7 2.0 %collective-permute-start.33 = (bf16[2,9,32,128]{3,2,1,0:T(8,128)(2,1)S(1)}, bf16[2,9,32,128]{3,2,1,0:T(8,128)(2,1)S(1)}, u32[]{:S(2)}, u32[]{:S(2)}) collective-permute-start(bf16[2,9,32,128]{3,2,1,0:T(8,128)(2,1)S(1)} %collective-permute-done.29.refs_3_), channel_id=1, source_target_pairs={{0,2},{1,5},{2,0},{3,7},{4,6},{5,1},{6,4},{7,3},{8,10},{9,13},{10,... | collective-permute-start | bytes 442376 | tf_op jit(solution)/shard_map/ppermute | solution.py:266
  84.7 1.5 %collective-permute-start.30 = (bf16[2,9,32,128]{3,2,1,0:T(8,128)(2,1)S(1)}, bf16[2,9,32,128]{3,2,1,0:T(8,128)(2,1)S(1)}, u32[]{:S(2)}, u32[]{:S(2)}) collective-permute-start(bf16[2,9,32,128]{3,2,1,0:T(8,128)(2,1)S(1)} %collective-permute-done.27.refs_1_), channel_id=1, source_target_pairs={{0,12},{1,11},{2,14},{3,9},{4,8},{5,15},{6,10},{7,13},{8,4},{9,3},... | collective-permute-start | bytes 442376 | tf_op jit(solution)/shard_map/ppermute | solution.py:266
  86.3 2.7 %collective-permute-done.33.refs_4_ = bf16[2,9,32,128]{3,2,1,0:T(8,128)(2,1)S(1)} collective-permute-done((bf16[2,9,32,128]{3,2,1,0:T(8,128)(2,1)S(1)}, bf16[2,9,32,128]{3,2,1,0:T(8,128)(2,1)S(1)}, u32[]{:S(2)}, u32[]{:S(2)}) %collective-permute-start.33) | collective-permute-done | bytes 147488 | tf_op jit(solution)/shard_map/ppermute | solution.py:266
  89.0 1.5 %collective-permute-done.31.refs_2_ = bf16[2,9,32,128]{3,2,1,0:T(8,128)(2,1)S(1)} collective-permute-done((bf16[2,9,32,128]{3,2,1,0:T(8,128)(2,1)S(1)}, bf16[2,9,32,128]{3,2,1,0:T(8,128)(2,1)S(1)}, u32[]{:S(2)}, u32[]{:S(2)}) %collective-permute-start.31) | collective-permute-done | bytes 147488 | tf_op jit(solution)/shard_map/ppermute | solution.py:266
  90.5 1.2 collective-permute-done.30.refs_1_
  91.7 0.5 collective-permute-start.36
  93.7 3.6 %shard_map.110 = (bf16[4,2,9,32,128]{4,3,2,1,0:T(8,128)(2,1)S(1)}, bf16[4,2,9,32,128]{4,3,2,1,0:T(8,128)(2,1)S(1)}, bf16[4,2,9,32,128]{4,3,2,1,0:T(8,128)(2,1)S(1)}, bf16[4,2,9,32,128]{4,3,2,1,0:T(8,128)(2,1)S(1)}) custom-call(s32[128]{0:T(128)S(1)} %bitcast.5, s32[128]{0:T(128)S(1)} %bitcast.7, bf16[128,96,96]{2,1,0:T(8,128)(2,1)S(1)} %copy-done.1, ...), custom_call_target="tpu_custom_call" | custom-call | flops 75497472 | bytes 10485760 | tf_op jit(solution)/shard_map/pallas_call | solution.py:403
  97.7 1.7 %collective-permute-done.39.swap_ref = bf16[4,2,9,32,128]{4,3,2,1,0:T(8,128)(2,1)S(1)} collective-permute-done((bf16[4,2,9,32,128]{4,3,2,1,0:T(8,128)(2,1)S(1)}, bf16[4,2,9,32,128]{4,3,2,1,0:T(8,128)(2,1)S(1)}, u32[]{:S(2)}, u32[]{:S(2)}) %collective-permute-start.39) | collective-permute-done | bytes 589856 | tf_op jit(solution)/shard_map/ppermute | solution.py:271
  99.9 1.1 collective-permute-start.40
  101.1 1.2 collective-permute-start.41
  102.3 1.5 %collective-permute-start.42 = (bf16[2,9,32,128]{3,2,1,0:T(8,128)(2,1)S(1)}, bf16[2,9,32,128]{3,2,1,0:T(8,128)(2,1)S(1)}, u32[]{:S(2)}, u32[]{:S(2)}) collective-permute-start(bf16[2,9,32,128]{3,2,1,0:T(8,128)(2,1)S(1)} %get-tuple-element.182), channel_id=1, source_target_pairs={{0,2},{1,5},{2,0},{3,7},{4,6},{5,1},{6,4},{7,3},{8,10},{9,13},{10,... | collective-permute-start | bytes 442376 | tf_op jit(solution)/shard_map/ppermute | solution.py:266
  104.0 1.8 %collective-permute-done.40.refs_0_ = bf16[2,9,32,128]{3,2,1,0:T(8,128)(2,1)S(1)} collective-permute-done((bf16[2,9,32,128]{3,2,1,0:T(8,128)(2,1)S(1)}, bf16[2,9,32,128]{3,2,1,0:T(8,128)(2,1)S(1)}, u32[]{:S(2)}, u32[]{:S(2)}) %collective-permute-start.40) | collective-permute-done | bytes 147488 | tf_op jit(solution)/shard_map/ppermute | solution.py:266
  105.9 0.8 collective-permute-done.41.refs_1_
  106.7 2.4 %collective-permute-done.42.refs_2_ = bf16[2,9,32,128]{3,2,1,0:T(8,128)(2,1)S(1)} collective-permute-done((bf16[2,9,32,128]{3,2,1,0:T(8,128)(2,1)S(1)}, bf16[2,9,32,128]{3,2,1,0:T(8,128)(2,1)S(1)}, u32[]{:S(2)}, u32[]{:S(2)}) %collective-permute-start.42) | collective-permute-done | bytes 147488 | tf_op jit(solution)/shard_map/ppermute | solution.py:266
  109.1 0.8 collective-permute-done.43.refs_3_
  110.1 0.9 collective-permute-start.45
  110.9 1.2 collective-permute-start.46
  112.2 1.7 %collective-permute-start.47 = (bf16[2,9,32,128]{3,2,1,0:T(8,128)(2,1)S(1)}, bf16[2,9,32,128]{3,2,1,0:T(8,128)(2,1)S(1)}, u32[]{:S(2)}, u32[]{:S(2)}) collective-permute-start(bf16[2,9,32,128]{3,2,1,0:T(8,128)(2,1)S(1)} %get-tuple-element.199), channel_id=1, source_target_pairs={{0,8},{1,3},{2,10},{3,1},{4,12},{5,7},{6,14},{7,5},{8,0},{9,11},{1... | collective-permute-start | bytes 442376 | tf_op jit(solution)/shard_map/ppermute | solution.py:266
  113.9 1.3 %collective-permute-start.48 = (bf16[1,32,256]{2,1,0:T(8,128)(2,1)S(1)}, bf16[1,32,256]{2,1,0:T(8,128)(2,1)S(1)}, u32[]{:S(2)}, u32[]{:S(2)}) collective-permute-start(bf16[1,32,256]{2,1,0:T(8,128)(2,1)S(1)} %get-tuple-element.201), channel_id=1, source_target_pairs={{1,3},{3,5},{5,7},{7,9},{9,11},{11,13},{13,15},{15,17},{17,19},{19... | collective-permute-start | bytes 49160 | tf_op jit(solution)/shard_map/ppermute | solution.py:414
  115.2 4.3 %collective-permute-done.48 = bf16[1,32,256]{2,1,0:T(8,128)(2,1)S(1)} collective-permute-done((bf16[1,32,256]{2,1,0:T(8,128)(2,1)S(1)}, bf16[1,32,256]{2,1,0:T(8,128)(2,1)S(1)}, u32[]{:S(2)}, u32[]{:S(2)}) %collective-permute-start.48) | collective-permute-done | bytes 16416 | tf_op jit(solution)/shard_map/ppermute | solution.py:414
  120.5 0.7 collective-permute-done.50.inner_ref
  121.5 3.9 %collective-permute-done.49.rest_0_ = bf16[9,32,128]{2,1,0:T(8,128)(2,1)S(1)} collective-permute-done((bf16[9,32,128]{2,1,0:T(8,128)(2,1)S(1)}, bf16[9,32,128]{2,1,0:T(8,128)(2,1)S(1)}, u32[]{:S(2)}, u32[]{:S(2)}) %collective-permute-start.49) | collective-permute-done | bytes 73760 | tf_op jit(solution)/shard_map/ppermute | solution.py:262
  125.5 1.6 %shard_map.115 = bf16[8,32,256]{2,1,0:T(8,128)(2,1)} custom-call(s32[12]{0:T(128)S(1)} %copy-done.8, f32[8,32,256]{2,1,0:T(8,128)S(1)} %shard_map.108.near_ref, f32[2,32,256]{2,1,0:T(8,128)S(1)} %shard_map.114.edge_ref, bf16[8,96,256]{2,1,0:T(8,128)(2,1)S(1)} %copy-done.2, bf16[8,96,96]{2,1,0:T(8,128)(2,1)S(1)} %copy-done.3, ...), custom_call_target="tpu_custom_call" | custom-call | tf_op jit(solution)/shard_map/pallas_call | solution.py:419
  (88 shorter events, 11.0 us)
Async XLA Ops:
  3.5 9.5 %copy-start.5 = (bf16[9,32,128]{2,1,0:T(8,128)(2,1)S(1)}, bf16[9,32,128]{2,1,0:T(8,128)(2,1)}, u32[]{:S(2)}) copy-start(bf16[9,32,128]{2,1,0:T(8,128)(2,1)} %get-tuple-element.107.__.refs_0_) | copy-start | bytes 221188
  3.5 15.0 %copy-start = (bf16[8,3,256,256]{3,2,1,0:T(8,128)(2,1)S(1)}, bf16[8,3,256,256]{3,2,1,0:T(8,128)(2,1)}, u32[]{:S(2)}) copy-start(bf16[8,3,256,256]{3,2,1,0:T(8,128)(2,1)} %last_ref.3) | copy-start | bytes 9437188
  3.6 15.0 %copy-start.4 = (bf16[8,32,256]{2,1,0:T(8,128)(2,1)S(1)}, bf16[8,32,256]{2,1,0:T(8,128)(2,1)}, u32[]{:S(2)}) copy-start(bf16[8,32,256]{2,1,0:T(8,128)(2,1)} %v_ref.1) | copy-start | bytes 393220
  3.6 9.5 %collective-permute-start = (bf16[9,32,128]{2,1,0:T(8,128)(2,1)}, bf16[9,32,128]{2,1,0:T(8,128)(2,1)S(1)}, u32[]{:S(2)}, u32[]{:S(2)}) collective-permute-start(bf16[9,32,128]{2,1,0:T(8,128)(2,1)} %get-tuple-element.107.__.refs_0_), channel_id=1, source_target_pairs={{0,16},{1,17},{2,18},{3,19},{4,20},{5,21},{6,22},{7,23},{8,24},{9,... | collective-permute-start | bytes 221192 | tf_op jit(solution)/shard_map/ppermute | solution.py:262
  13.0 21.9 %copy-start.1 = (bf16[128,96,96]{2,1,0:T(8,128)(2,1)S(1)}, bf16[128,96,96]{2,1,0:T(8,128)(2,1)}, u32[]{:S(2)}) copy-start(bf16[128,96,96]{2,1,0:T(8,128)(2,1)} %copy.10._.coupling_ref) | copy-start | bytes 7077892
  13.9 19.7 %copy-start.9 = (s32[128]{0:T(128)S(1)}, s32[128]{0:T(128)}, u32[]{:S(2)}) copy-start(s32[128]{0:T(128)} %param.14) | copy-start | bytes 1540
  13.9 19.7 %copy-start.10 = (s32[128]{0:T(128)S(1)}, s32[128]{0:T(128)}, u32[]{:S(2)}) copy-start(s32[128]{0:T(128)} %param.15) | copy-start | bytes 1540
  13.9 6.6 %collective-permute-start.3 = (bf16[2,9,32,128]{3,2,1,0:T(8,128)(2,1)S(1)}, bf16[2,9,32,128]{3,2,1,0:T(8,128)(2,1)S(1)}, u32[]{:S(2)}, u32[]{:S(2)}) collective-permute-start(bf16[2,9,32,128]{3,2,1,0:T(8,128)(2,1)S(1)} %shard_map.97.refs_0_), channel_id=1, source_target_pairs={{0,8},{1,3},{2,10},{3,1},{4,12},{5,7},{6,14},{7,5},{8,0},{9,11},{1... | collective-permute-start | bytes 442376 | tf_op jit(solution)/shard_map/ppermute | solution.py:266
  15.5 6.2 %collective-permute-start.2 = (bf16[2,9,32,128]{3,2,1,0:T(8,128)(2,1)S(1)}, bf16[2,9,32,128]{3,2,1,0:T(8,128)(2,1)S(1)}, u32[]{:S(2)}, u32[]{:S(2)}) collective-permute-start(bf16[2,9,32,128]{3,2,1,0:T(8,128)(2,1)S(1)} %shard_map.97.refs_0_), channel_id=1, source_target_pairs={{0,4},{1,9},{2,6},{3,11},{4,0},{5,13},{6,2},{7,15},{8,12},{9,1},{1... | collective-permute-start | bytes 442376 | tf_op jit(solution)/shard_map/ppermute | solution.py:266
  17.0 5.1 %collective-permute-start.1 = (bf16[2,9,32,128]{3,2,1,0:T(8,128)(2,1)S(1)}, bf16[2,9,32,128]{3,2,1,0:T(8,128)(2,1)S(1)}, u32[]{:S(2)}, u32[]{:S(2)}) collective-permute-start(bf16[2,9,32,128]{3,2,1,0:T(8,128)(2,1)S(1)} %shard_map.97.refs_0_), channel_id=1, source_target_pairs={{0,2},{1,5},{2,0},{3,7},{4,6},{5,1},{6,4},{7,3},{8,10},{9,13},{10,... | collective-permute-start | bytes 442376 | tf_op jit(solution)/shard_map/ppermute | solution.py:266
  22.2 10.3 %collective-permute-start.8 = (bf16[4,2,9,32,128]{4,3,2,1,0:T(8,128)(2,1)S(1)}, bf16[4,2,9,32,128]{4,3,2,1,0:T(8,128)(2,1)S(1)}, u32[]{:S(2)}, u32[]{:S(2)}) collective-permute-start(bf16[4,2,9,32,128]{4,3,2,1,0:T(8,128)(2,1)S(1)} %shard_map.100.refs_0_), channel_id=1, source_target_pairs={{0,1},{1,0},{2,3},{3,2},{4,5},{5,4},{6,7},{7,6},{8,9},{9,8},{10,11... | collective-permute-start | bytes 1769480 | tf_op jit(solution)/shard_map/ppermute | solution.py:271
  22.3 5.9 %collective-permute-start.6 = (bf16[2,9,32,128]{3,2,1,0:T(8,128)(2,1)S(1)}, bf16[2,9,32,128]{3,2,1,0:T(8,128)(2,1)S(1)}, u32[]{:S(2)}, u32[]{:S(2)}) collective-permute-start(bf16[2,9,32,128]{3,2,1,0:T(8,128)(2,1)S(1)} %collective-permute-done.2.refs_2_), channel_id=1, source_target_pairs={{0,8},{1,3},{2,10},{3,1},{4,12},{5,7},{6,14},{7,5},{8,0},{9,11},{1... | collective-permute-start | bytes 442376 | tf_op jit(solution)/shard_map/ppermute | solution.py:266
  22.8 5.7 %collective-permute-start.7 = (bf16[2,9,32,128]{3,2,1,0:T(8,128)(2,1)S(1)}, bf16[2,9,32,128]{3,2,1,0:T(8,128)(2,1)S(1)}, u32[]{:S(2)}, u32[]{:S(2)}) collective-permute-start(bf16[2,9,32,128]{3,2,1,0:T(8,128)(2,1)S(1)} %collective-permute-done.3.refs_3_), channel_id=1, source_target_pairs={{0,2},{1,5},{2,0},{3,7},{4,6},{5,1},{6,4},{7,3},{8,10},{9,13},{10,... | collective-permute-start | bytes 442376 | tf_op jit(solution)/shard_map/ppermute | solution.py:266
  24.3 5.9 %collective-permute-start.5 = (bf16[2,9,32,128]{3,2,1,0:T(8,128)(2,1)S(1)}, bf16[2,9,32,128]{3,2,1,0:T(8,128)(2,1)S(1)}, u32[]{:S(2)}, u32[]{:S(2)}) collective-permute-start(bf16[2,9,32,128]{3,2,1,0:T(8,128)(2,1)S(1)} %collective-permute-done.1.refs_1_), channel_id=1, source_target_pairs={{0,4},{1,9},{2,6},{3,11},{4,0},{5,13},{6,2},{7,15},{8,12},{9,1},{1... | collective-permute-start | bytes 442376 | tf_op jit(solution)/shard_map/ppermute | solution.py:266
  24.8 7.7 %collective-permute-start.4 = (bf16[2,9,32,128]{3,2,1,0:T(8,128)(2,1)S(1)}, bf16[2,9,32,128]{3,2,1,0:T(8,128)(2,1)S(1)}, u32[]{:S(2)}, u32[]{:S(2)}) collective-permute-start(bf16[2,9,32,128]{3,2,1,0:T(8,128)(2,1)S(1)} %collective-permute-done.1.refs_1_), channel_id=1, source_target_pairs={{0,12},{1,11},{2,14},{3,9},{4,8},{5,15},{6,10},{7,13},{8,4},{9,3},... | collective-permute-start | bytes 442376 | tf_op jit(solution)/shard_map/ppermute | solution.py:266
  32.5 1.5 %collective-permute-start.9 = (bf16[2,9,32,128]{3,2,1,0:T(8,128)(2,1)S(1)}, bf16[2,9,32,128]{3,2,1,0:T(8,128)(2,1)S(1)}, u32[]{:S(2)}, u32[]{:S(2)}) collective-permute-start(bf16[2,9,32,128]{3,2,1,0:T(8,128)(2,1)S(1)} %collective-permute-done.4.refs_1_), channel_id=1, source_target_pairs={{0,1},{1,0},{2,3},{3,2},{4,5},{5,4},{6,7},{7,6},{8,9},{9,8},{10,11... | collective-permute-start | bytes 442376 | tf_op jit(solution)/shard_map/ppermute | solution.py:271
  33.0 1.4 %collective-permute-start.10 = (bf16[2,9,32,128]{3,2,1,0:T(8,128)(2,1)S(1)}, bf16[2,9,32,128]{3,2,1,0:T(8,128)(2,1)S(1)}, u32[]{:S(2)}, u32[]{:S(2)}) collective-permute-start(bf16[2,9,32,128]{3,2,1,0:T(8,128)(2,1)S(1)} %collective-permute-done.5.refs_2_), channel_id=1, source_target_pairs={{0,1},{1,0},{2,3},{3,2},{4,5},{5,4},{6,7},{7,6},{8,9},{9,8},{10,11... | collective-permute-start | bytes 442376 | tf_op jit(solution)/shard_map/ppermute | solution.py:271
  33.0 1.6 %collective-permute-start.11 = (bf16[2,9,32,128]{3,2,1,0:T(8,128)(2,1)S(1)}, bf16[2,9,32,128]{3,2,1,0:T(8,128)(2,1)S(1)}, u32[]{:S(2)}, u32[]{:S(2)}) collective-permute-start(bf16[2,9,32,128]{3,2,1,0:T(8,128)(2,1)S(1)} %collective-permute-done.6.refs_3_), channel_id=1, source_target_pairs={{0,1},{1,0},{2,3},{3,2},{4,5},{5,4},{6,7},{7,6},{8,9},{9,8},{10,11... | collective-permute-start | bytes 442376 | tf_op jit(solution)/shard_map/ppermute | solution.py:271
  33.5 1.4 %collective-permute-start.12 = (bf16[2,9,32,128]{3,2,1,0:T(8,128)(2,1)S(1)}, bf16[2,9,32,128]{3,2,1,0:T(8,128)(2,1)S(1)}, u32[]{:S(2)}, u32[]{:S(2)}) collective-permute-start(bf16[2,9,32,128]{3,2,1,0:T(8,128)(2,1)S(1)} %collective-permute-done.7.refs_4_), channel_id=1, source_target_pairs={{0,1},{1,0},{2,3},{3,2},{4,5},{5,4},{6,7},{7,6},{8,9},{9,8},{10,11... | collective-permute-start | bytes 442376 | tf_op jit(solution)/shard_map/ppermute | solution.py:271
  34.9 19.1 %copy-start.12 = (bf16[1,32,256]{2,1,0:T(8,128)(2,1)S(1)}, bf16[1,32,256]{2,1,0:T(8,128)(2,1)}, u32[]{:S(2)}) copy-start(bf16[1,32,256]{2,1,0:T(8,128)(2,1)} %get-tuple-element.149) | copy-start | bytes 49156
  38.5 22.5 %copy-start.11 = (bf16[1,32,256]{2,1,0:T(8,128)(2,1)S(1)}, bf16[1,32,256]{2,1,0:T(8,128)(2,1)}, u32[]{:S(2)}) copy-start(bf16[1,32,256]{2,1,0:T(8,128)(2,1)} %get-tuple-element.155) | copy-start | bytes 49156
  38.5 2.1 %collective-permute-start.13 = (bf16[4,2,9,32,128]{4,3,2,1,0:T(8,128)(2,1)S(1)}, bf16[4,2,9,32,128]{4,3,2,1,0:T(8,128)(2,1)S(1)}, u32[]{:S(2)}, u32[]{:S(2)}) collective-permute-start(bf16[4,2,9,32,128]{4,3,2,1,0:T(8,128)(2,1)S(1)} %get-tuple-element.122), channel_id=1, source_target_pairs={{0,1},{1,0},{2,3},{3,2},{4,5},{5,4},{6,7},{7,6},{8,9},{9,8},{10,11... | collective-permute-start | bytes 1769480 | tf_op jit(solution)/shard_map/ppermute | solution.py:271
  40.7 10.0 %collective-permute-start.18 = (bf16[4,2,9,32,128]{4,3,2,1,0:T(8,128)(2,1)S(1)}, bf16[4,2,9,32,128]{4,3,2,1,0:T(8,128)(2,1)S(1)}, u32[]{:S(2)}, u32[]{:S(2)}) collective-permute-start(bf16[4,2,9,32,128]{4,3,2,1,0:T(8,128)(2,1)S(1)} %get-tuple-element.132), channel_id=1, source_target_pairs={{0,1},{1,0},{2,3},{3,2},{4,5},{5,4},{6,7},{7,6},{8,9},{9,8},{10,11... | collective-permute-start | bytes 1769480 | tf_op jit(solution)/shard_map/ppermute | solution.py:271
  41.0 6.6 %collective-permute-start.14 = (bf16[2,9,32,128]{3,2,1,0:T(8,128)(2,1)S(1)}, bf16[2,9,32,128]{3,2,1,0:T(8,128)(2,1)S(1)}, u32[]{:S(2)}, u32[]{:S(2)}) collective-permute-start(bf16[2,9,32,128]{3,2,1,0:T(8,128)(2,1)S(1)} %get-tuple-element.128), channel_id=1, source_target_pairs={{0,4},{1,9},{2,6},{3,11},{4,0},{5,13},{6,2},{7,15},{8,12},{9,1},{1... | collective-permute-start | bytes 442376 | tf_op jit(solution)/shard_map/ppermute | solution.py:266
  42.0 6.4 %collective-permute-start.15 = (bf16[2,9,32,128]{3,2,1,0:T(8,128)(2,1)S(1)}, bf16[2,9,32,128]{3,2,1,0:T(8,128)(2,1)S(1)}, u32[]{:S(2)}, u32[]{:S(2)}) collective-permute-start(bf16[2,9,32,128]{3,2,1,0:T(8,128)(2,1)S(1)} %get-tuple-element.129), channel_id=1, source_target_pairs={{0,8},{1,3},{2,10},{3,1},{4,12},{5,7},{6,14},{7,5},{8,0},{9,11},{1... | collective-permute-start | bytes 442376 | tf_op jit(solution)/shard_map/ppermute | solution.py:266
  42.5 6.0 %collective-permute-start.16 = (bf16[2,9,32,128]{3,2,1,0:T(8,128)(2,1)S(1)}, bf16[2,9,32,128]{3,2,1,0:T(8,128)(2,1)S(1)}, u32[]{:S(2)}, u32[]{:S(2)}) collective-permute-start(bf16[2,9,32,128]{3,2,1,0:T(8,128)(2,1)S(1)} %get-tuple-element.130), channel_id=1, source_target_pairs={{0,2},{1,5},{2,0},{3,7},{4,6},{5,1},{6,4},{7,3},{8,10},{9,13},{10,... | collective-permute-start | bytes 442376 | tf_op jit(solution)/shard_map/ppermute | solution.py:266
  44.0 6.8 %collective-permute-start.17 = (bf16[2,9,32,128]{3,2,1,0:T(8,128)(2,1)S(1)}, bf16[2,9,32,128]{3,2,1,0:T(8,128)(2,1)S(1)}, u32[]{:S(2)}, u32[]{:S(2)}) collective-permute-start(bf16[2,9,32,128]{3,2,1,0:T(8,128)(2,1)S(1)} %get-tuple-element.131), channel_id=1, source_target_pairs={{0,12},{1,11},{2,14},{3,9},{4,8},{5,15},{6,10},{7,13},{8,4},{9,3},... | collective-permute-start | bytes 442376 | tf_op jit(solution)/shard_map/ppermute | solution.py:266
  51.0 8.6 %collective-permute-start.19 = (bf16[2,9,32,128]{3,2,1,0:T(8,128)(2,1)S(1)}, bf16[2,9,32,128]{3,2,1,0:T(8,128)(2,1)S(1)}, u32[]{:S(2)}, u32[]{:S(2)}) collective-permute-start(bf16[2,9,32,128]{3,2,1,0:T(8,128)(2,1)S(1)} %get-tuple-element.145), channel_id=1, source_target_pairs={{0,2},{1,5},{2,0},{3,7},{4,6},{5,1},{6,4},{7,3},{8,10},{9,13},{10,... | collective-permute-start | bytes 442376 | tf_op jit(solution)/shard_map/ppermute | solution.py:266
  52.0 7.7 %collective-permute-start.20 = (bf16[2,9,32,128]{3,2,1,0:T(8,128)(2,1)S(1)}, bf16[2,9,32,128]{3,2,1,0:T(8,128)(2,1)S(1)}, u32[]{:S(2)}, u32[]{:S(2)}) collective-permute-start(bf16[2,9,32,128]{3,2,1,0:T(8,128)(2,1)S(1)} %get-tuple-element.146), channel_id=1, source_target_pairs={{0,4},{1,9},{2,6},{3,11},{4,0},{5,13},{6,2},{7,15},{8,12},{9,1},{1... | collective-permute-start | bytes 442376 | tf_op jit(solution)/shard_map/ppermute | solution.py:266
  53.1 6.6 %collective-permute-start.21 = (bf16[2,9,32,128]{3,2,1,0:T(8,128)(2,1)S(1)}, bf16[2,9,32,128]{3,2,1,0:T(8,128)(2,1)S(1)}, u32[]{:S(2)}, u32[]{:S(2)}) collective-permute-start(bf16[2,9,32,128]{3,2,1,0:T(8,128)(2,1)S(1)} %get-tuple-element.147), channel_id=1, source_target_pairs={{0,8},{1,3},{2,10},{3,1},{4,12},{5,7},{6,14},{7,5},{8,0},{9,11},{1... | collective-permute-start | bytes 442376 | tf_op jit(solution)/shard_map/ppermute | solution.py:266
  54.0 5.6 %collective-permute-start.22 = (bf16[1,32,256]{2,1,0:T(8,128)(2,1)S(1)}, bf16[1,32,256]{2,1,0:T(8,128)(2,1)S(1)}, u32[]{:S(2)}, u32[]{:S(2)}) collective-permute-start(bf16[1,32,256]{2,1,0:T(8,128)(2,1)S(1)} %copy-done.12), channel_id=1, source_target_pairs={{1,3},{3,5},{5,7},{7,9},{9,11},{11,13},{13,15},{15,17},{17,19},{19... | collective-permute-start | bytes 49160 | tf_op jit(solution)/shard_map/ppermute | solution.py:414
  59.7 6.1 %copy-start.2 = (bf16[8,96,256]{2,1,0:T(8,128)(2,1)S(1)}, bf16[8,96,256]{2,1,0:T(8,128)(2,1)}, u32[]{:S(2)}) copy-start(bf16[8,96,256]{2,1,0:T(8,128)(2,1)} %basis_ref.3) | copy-start | bytes 1179652
  59.7 6.1 %copy-start.3 = (bf16[8,96,96]{2,1,0:T(8,128)(2,1)S(1)}, bf16[8,96,96]{2,1,0:T(8,128)(2,1)}, u32[]{:S(2)}) copy-start(bf16[8,96,96]{2,1,0:T(8,128)(2,1)} %transfer_ref.3) | copy-start | bytes 442372
  59.7 6.1 %copy-start.8 = (s32[12]{0:T(128)S(1)}, s32[12]{0:T(128)}, u32[]{:S(2)}) copy-start(s32[12]{0:T(128)} %ranks_ref.5) | copy-start | bytes 148
  59.8 6.1 %collective-permute-start.23 = (bf16[9,32,128]{2,1,0:T(8,128)(2,1)S(1)}, bf16[9,32,128]{2,1,0:T(8,128)(2,1)S(1)}, u32[]{:S(2)}, u32[]{:S(2)}) collective-permute-start(bf16[9,32,128]{2,1,0:T(8,128)(2,1)S(1)} %get-tuple-element.154), channel_id=1, source_target_pairs={{0,16},{1,17},{2,18},{3,19},{4,20},{5,21},{6,22},{7,23},{8,24},{9,... | collective-permute-start | bytes 221192 | tf_op jit(solution)/shard_map/ppermute | solution.py:262
  61.0 1.2 collective-permute-start.24
  61.0 1.3 %collective-permute-start.25 = (bf16[1,32,256]{2,1,0:T(8,128)(2,1)S(1)}, bf16[1,32,256]{2,1,0:T(8,128)(2,1)S(1)}, u32[]{:S(2)}, u32[]{:S(2)}) collective-permute-start(bf16[1,32,256]{2,1,0:T(8,128)(2,1)S(1)} %collective-permute-done.22), channel_id=1, source_target_pairs={{0,1},{1,0},{2,3},{3,2},{4,5},{5,4},{6,7},{7,6},{8,9},{9,8},{10,11... | collective-permute-start | bytes 49160 | tf_op jit(solution)/shard_map/ppermute | solution.py:271
  67.5 6.0 %collective-permute-start.26 = (bf16[9,32,128]{2,1,0:T(8,128)(2,1)S(1)}, bf16[9,32,128]{2,1,0:T(8,128)(2,1)S(1)}, u32[]{:S(2)}, u32[]{:S(2)}) collective-permute-start(bf16[9,32,128]{2,1,0:T(8,128)(2,1)S(1)} %get-tuple-element.161.refs_0_), channel_id=1, source_target_pairs={{0,16},{1,17},{2,18},{3,19},{4,20},{5,21},{6,22},{7,23},{8,24},{9,... | collective-permute-start | bytes 221192 | tf_op jit(solution)/shard_map/ppermute | solution.py:262
  73.5 5.5 %collective-permute-start.29 = (bf16[2,9,32,128]{3,2,1,0:T(8,128)(2,1)S(1)}, bf16[2,9,32,128]{3,2,1,0:T(8,128)(2,1)S(1)}, u32[]{:S(2)}, u32[]{:S(2)}) collective-permute-start(bf16[2,9,32,128]{3,2,1,0:T(8,128)(2,1)S(1)} %shard_map.107.refs_0_), channel_id=1, source_target_pairs={{0,8},{1,3},{2,10},{3,1},{4,12},{5,7},{6,14},{7,5},{8,0},{9,11},{1... | collective-permute-start | bytes 442376 | tf_op jit(solution)/shard_map/ppermute | solution.py:266
  73.6 5.4 %collective-permute-start.28 = (bf16[2,9,32,128]{3,2,1,0:T(8,128)(2,1)S(1)}, bf16[2,9,32,128]{3,2,1,0:T(8,128)(2,1)S(1)}, u32[]{:S(2)}, u32[]{:S(2)}) collective-permute-start(bf16[2,9,32,128]{3,2,1,0:T(8,128)(2,1)S(1)} %shard_map.107.refs_0_), channel_id=1, source_target_pairs={{0,4},{1,9},{2,6},{3,11},{4,0},{5,13},{6,2},{7,15},{8,12},{9,1},{1... | collective-permute-start | bytes 442376 | tf_op jit(solution)/shard_map/ppermute | solution.py:266
  74.4 6.1 %collective-permute-start.27 = (bf16[2,9,32,128]{3,2,1,0:T(8,128)(2,1)S(1)}, bf16[2,9,32,128]{3,2,1,0:T(8,128)(2,1)S(1)}, u32[]{:S(2)}, u32[]{:S(2)}) collective-permute-start(bf16[2,9,32,128]{3,2,1,0:T(8,128)(2,1)S(1)} %shard_map.107.refs_0_), channel_id=1, source_target_pairs={{0,2},{1,5},{2,0},{3,7},{4,6},{5,1},{6,4},{7,3},{8,10},{9,13},{10,... | collective-permute-start | bytes 442376 | tf_op jit(solution)/shard_map/ppermute | solution.py:266
  77.4 0.9 copy-start.6
  80.6 11.0 %collective-permute-start.34 = (bf16[4,2,9,32,128]{4,3,2,1,0:T(8,128)(2,1)S(1)}, bf16[4,2,9,32,128]{4,3,2,1,0:T(8,128)(2,1)S(1)}, u32[]{:S(2)}, u32[]{:S(2)}) collective-permute-start(bf16[4,2,9,32,128]{4,3,2,1,0:T(8,128)(2,1)S(1)} %shard_map.109.refs_0_), channel_id=1, source_target_pairs={{0,1},{1,0},{2,3},{3,2},{4,5},{5,4},{6,7},{7,6},{8,9},{9,8},{10,11... | collective-permute-start | bytes 1769480 | tf_op jit(solution)/shard_map/ppermute | solution.py:271
  80.7 5.6 %collective-permute-start.32 = (bf16[2,9,32,128]{3,2,1,0:T(8,128)(2,1)S(1)}, bf16[2,9,32,128]{3,2,1,0:T(8,128)(2,1)S(1)}, u32[]{:S(2)}, u32[]{:S(2)}) collective-permute-start(bf16[2,9,32,128]{3,2,1,0:T(8,128)(2,1)S(1)} %collective-permute-done.28.refs_2_), channel_id=1, source_target_pairs={{0,8},{1,3},{2,10},{3,1},{4,12},{5,7},{6,14},{7,5},{8,0},{9,11},{1... | collective-permute-start | bytes 442376 | tf_op jit(solution)/shard_map/ppermute | solution.py:266
  82.7 6.3 %collective-permute-start.33 = (bf16[2,9,32,128]{3,2,1,0:T(8,128)(2,1)S(1)}, bf16[2,9,32,128]{3,2,1,0:T(8,128)(2,1)S(1)}, u32[]{:S(2)}, u32[]{:S(2)}) collective-permute-start(bf16[2,9,32,128]{3,2,1,0:T(8,128)(2,1)S(1)} %collective-permute-done.29.refs_3_), channel_id=1, source_target_pairs={{0,2},{1,5},{2,0},{3,7},{4,6},{5,1},{6,4},{7,3},{8,10},{9,13},{10,... | collective-permute-start | bytes 442376 | tf_op jit(solution)/shard_map/ppermute | solution.py:266
  84.7 5.7 %collective-permute-start.31 = (bf16[2,9,32,128]{3,2,1,0:T(8,128)(2,1)S(1)}, bf16[2,9,32,128]{3,2,1,0:T(8,128)(2,1)S(1)}, u32[]{:S(2)}, u32[]{:S(2)}) collective-permute-start(bf16[2,9,32,128]{3,2,1,0:T(8,128)(2,1)S(1)} %collective-permute-done.27.refs_1_), channel_id=1, source_target_pairs={{0,4},{1,9},{2,6},{3,11},{4,0},{5,13},{6,2},{7,15},{8,12},{9,1},{1... | collective-permute-start | bytes 442376 | tf_op jit(solution)/shard_map/ppermute | solution.py:266
  84.7 6.9 %collective-permute-start.30 = (bf16[2,9,32,128]{3,2,1,0:T(8,128)(2,1)S(1)}, bf16[2,9,32,128]{3,2,1,0:T(8,128)(2,1)S(1)}, u32[]{:S(2)}, u32[]{:S(2)}) collective-permute-start(bf16[2,9,32,128]{3,2,1,0:T(8,128)(2,1)S(1)} %collective-permute-done.27.refs_1_), channel_id=1, source_target_pairs={{0,12},{1,11},{2,14},{3,9},{4,8},{5,15},{6,10},{7,13},{8,4},{9,3},... | collective-permute-start | bytes 442376 | tf_op jit(solution)/shard_map/ppermute | solution.py:266
  91.6 1.4 %collective-permute-start.35 = (bf16[2,9,32,128]{3,2,1,0:T(8,128)(2,1)S(1)}, bf16[2,9,32,128]{3,2,1,0:T(8,128)(2,1)S(1)}, u32[]{:S(2)}, u32[]{:S(2)}) collective-permute-start(bf16[2,9,32,128]{3,2,1,0:T(8,128)(2,1)S(1)} %collective-permute-done.30.refs_1_), channel_id=1, source_target_pairs={{0,1},{1,0},{2,3},{3,2},{4,5},{5,4},{6,7},{7,6},{8,9},{9,8},{10,11... | collective-permute-start | bytes 442376 | tf_op jit(solution)/shard_map/ppermute | solution.py:271
  91.7 1.6 %collective-permute-start.36 = (bf16[2,9,32,128]{3,2,1,0:T(8,128)(2,1)S(1)}, bf16[2,9,32,128]{3,2,1,0:T(8,128)(2,1)S(1)}, u32[]{:S(2)}, u32[]{:S(2)}) collective-permute-start(bf16[2,9,32,128]{3,2,1,0:T(8,128)(2,1)S(1)} %collective-permute-done.31.refs_2_), channel_id=1, source_target_pairs={{0,1},{1,0},{2,3},{3,2},{4,5},{5,4},{6,7},{7,6},{8,9},{9,8},{10,11... | collective-permute-start | bytes 442376 | tf_op jit(solution)/shard_map/ppermute | solution.py:271
  92.2 1.4 %collective-permute-start.37 = (bf16[2,9,32,128]{3,2,1,0:T(8,128)(2,1)S(1)}, bf16[2,9,32,128]{3,2,1,0:T(8,128)(2,1)S(1)}, u32[]{:S(2)}, u32[]{:S(2)}) collective-permute-start(bf16[2,9,32,128]{3,2,1,0:T(8,128)(2,1)S(1)} %collective-permute-done.32.refs_3_), channel_id=1, source_target_pairs={{0,1},{1,0},{2,3},{3,2},{4,5},{5,4},{6,7},{7,6},{8,9},{9,8},{10,11... | collective-permute-start | bytes 442376 | tf_op jit(solution)/shard_map/ppermute | solution.py:271
  92.2 1.6 %collective-permute-start.38 = (bf16[2,9,32,128]{3,2,1,0:T(8,128)(2,1)S(1)}, bf16[2,9,32,128]{3,2,1,0:T(8,128)(2,1)S(1)}, u32[]{:S(2)}, u32[]{:S(2)}) collective-permute-start(bf16[2,9,32,128]{3,2,1,0:T(8,128)(2,1)S(1)} %collective-permute-done.33.refs_4_), channel_id=1, source_target_pairs={{0,1},{1,0},{2,3},{3,2},{4,5},{5,4},{6,7},{7,6},{8,9},{9,8},{10,11... | collective-permute-start | bytes 442376 | tf_op jit(solution)/shard_map/ppermute | solution.py:271
  97.4 2.1 %collective-permute-start.39 = (bf16[4,2,9,32,128]{4,3,2,1,0:T(8,128)(2,1)S(1)}, bf16[4,2,9,32,128]{4,3,2,1,0:T(8,128)(2,1)S(1)}, u32[]{:S(2)}, u32[]{:S(2)}) collective-permute-start(bf16[4,2,9,32,128]{4,3,2,1,0:T(8,128)(2,1)S(1)} %get-tuple-element.174), channel_id=1, source_target_pairs={{0,1},{1,0},{2,3},{3,2},{4,5},{5,4},{6,7},{7,6},{8,9},{9,8},{10,11... | collective-permute-start | bytes 1769480 | tf_op jit(solution)/shard_map/ppermute | solution.py:271
  99.6 10.3 %collective-permute-start.44 = (bf16[4,2,9,32,128]{4,3,2,1,0:T(8,128)(2,1)S(1)}, bf16[4,2,9,32,128]{4,3,2,1,0:T(8,128)(2,1)S(1)}, u32[]{:S(2)}, u32[]{:S(2)}) collective-permute-start(bf16[4,2,9,32,128]{4,3,2,1,0:T(8,128)(2,1)S(1)} %get-tuple-element.184), channel_id=1, source_target_pairs={{0,1},{1,0},{2,3},{3,2},{4,5},{5,4},{6,7},{7,6},{8,9},{9,8},{10,11... | collective-permute-start | bytes 1769480 | tf_op jit(solution)/shard_map/ppermute | solution.py:271
  99.9 5.9 %collective-permute-start.40 = (bf16[2,9,32,128]{3,2,1,0:T(8,128)(2,1)S(1)}, bf16[2,9,32,128]{3,2,1,0:T(8,128)(2,1)S(1)}, u32[]{:S(2)}, u32[]{:S(2)}) collective-permute-start(bf16[2,9,32,128]{3,2,1,0:T(8,128)(2,1)S(1)} %get-tuple-element.180), channel_id=1, source_target_pairs={{0,4},{1,9},{2,6},{3,11},{4,0},{5,13},{6,2},{7,15},{8,12},{9,1},{1... | collective-permute-start | bytes 442376 | tf_op jit(solution)/shard_map/ppermute | solution.py:266
  101.1 5.6 %collective-permute-start.41 = (bf16[2,9,32,128]{3,2,1,0:T(8,128)(2,1)S(1)}, bf16[2,9,32,128]{3,2,1,0:T(8,128)(2,1)S(1)}, u32[]{:S(2)}, u32[]{:S(2)}) collective-permute-start(bf16[2,9,32,128]{3,2,1,0:T(8,128)(2,1)S(1)} %get-tuple-element.181), channel_id=1, source_target_pairs={{0,8},{1,3},{2,10},{3,1},{4,12},{5,7},{6,14},{7,5},{8,0},{9,11},{1... | collective-permute-start | bytes 442376 | tf_op jit(solution)/shard_map/ppermute | solution.py:266
  102.3 6.7 %collective-permute-start.42 = (bf16[2,9,32,128]{3,2,1,0:T(8,128)(2,1)S(1)}, bf16[2,9,32,128]{3,2,1,0:T(8,128)(2,1)S(1)}, u32[]{:S(2)}, u32[]{:S(2)}) collective-permute-start(bf16[2,9,32,128]{3,2,1,0:T(8,128)(2,1)S(1)} %get-tuple-element.182), channel_id=1, source_target_pairs={{0,2},{1,5},{2,0},{3,7},{4,6},{5,1},{6,4},{7,3},{8,10},{9,13},{10,... | collective-permute-start | bytes 442376 | tf_op jit(solution)/shard_map/ppermute | solution.py:266
  103.8 6.0 %collective-permute-start.43 = (bf16[2,9,32,128]{3,2,1,0:T(8,128)(2,1)S(1)}, bf16[2,9,32,128]{3,2,1,0:T(8,128)(2,1)S(1)}, u32[]{:S(2)}, u32[]{:S(2)}) collective-permute-start(bf16[2,9,32,128]{3,2,1,0:T(8,128)(2,1)S(1)} %get-tuple-element.183), channel_id=1, source_target_pairs={{0,12},{1,11},{2,14},{3,9},{4,8},{5,15},{6,10},{7,13},{8,4},{9,3},... | collective-permute-start | bytes 442376 | tf_op jit(solution)/shard_map/ppermute | solution.py:266
  110.1 9.4 %collective-permute-start.45 = (bf16[2,9,32,128]{3,2,1,0:T(8,128)(2,1)S(1)}, bf16[2,9,32,128]{3,2,1,0:T(8,128)(2,1)S(1)}, u32[]{:S(2)}, u32[]{:S(2)}) collective-permute-start(bf16[2,9,32,128]{3,2,1,0:T(8,128)(2,1)S(1)} %get-tuple-element.197), channel_id=1, source_target_pairs={{0,2},{1,5},{2,0},{3,7},{4,6},{5,1},{6,4},{7,3},{8,10},{9,13},{10,... | collective-permute-start | bytes 442376 | tf_op jit(solution)/shard_map/ppermute | solution.py:266
  110.9 8.5 %collective-permute-start.46 = (bf16[2,9,32,128]{3,2,1,0:T(8,128)(2,1)S(1)}, bf16[2,9,32,128]{3,2,1,0:T(8,128)(2,1)S(1)}, u32[]{:S(2)}, u32[]{:S(2)}) collective-permute-start(bf16[2,9,32,128]{3,2,1,0:T(8,128)(2,1)S(1)} %get-tuple-element.198), channel_id=1, source_target_pairs={{0,4},{1,9},{2,6},{3,11},{4,0},{5,13},{6,2},{7,15},{8,12},{9,1},{1... | collective-permute-start | bytes 442376 | tf_op jit(solution)/shard_map/ppermute | solution.py:266
  112.2 7.3 %collective-permute-start.47 = (bf16[2,9,32,128]{3,2,1,0:T(8,128)(2,1)S(1)}, bf16[2,9,32,128]{3,2,1,0:T(8,128)(2,1)S(1)}, u32[]{:S(2)}, u32[]{:S(2)}) collective-permute-start(bf16[2,9,32,128]{3,2,1,0:T(8,128)(2,1)S(1)} %get-tuple-element.199), channel_id=1, source_target_pairs={{0,8},{1,3},{2,10},{3,1},{4,12},{5,7},{6,14},{7,5},{8,0},{9,11},{1... | collective-permute-start | bytes 442376 | tf_op jit(solution)/shard_map/ppermute | solution.py:266
  113.9 5.6 %collective-permute-start.48 = (bf16[1,32,256]{2,1,0:T(8,128)(2,1)S(1)}, bf16[1,32,256]{2,1,0:T(8,128)(2,1)S(1)}, u32[]{:S(2)}, u32[]{:S(2)}) collective-permute-start(bf16[1,32,256]{2,1,0:T(8,128)(2,1)S(1)} %get-tuple-element.201), channel_id=1, source_target_pairs={{1,3},{3,5},{5,7},{7,9},{9,11},{11,13},{13,15},{15,17},{17,19},{19... | collective-permute-start | bytes 49160 | tf_op jit(solution)/shard_map/ppermute | solution.py:414
  119.6 5.9 %collective-permute-start.49 = (bf16[9,32,128]{2,1,0:T(8,128)(2,1)S(1)}, bf16[9,32,128]{2,1,0:T(8,128)(2,1)S(1)}, u32[]{:S(2)}, u32[]{:S(2)}) collective-permute-start(bf16[9,32,128]{2,1,0:T(8,128)(2,1)S(1)} %get-tuple-element.206), channel_id=1, source_target_pairs={{0,16},{1,17},{2,18},{3,19},{4,20},{5,21},{6,22},{7,23},{8,24},{9,... | collective-permute-start | bytes 221192 | tf_op jit(solution)/shard_map/ppermute | solution.py:262
  120.0 1.2 collective-permute-start.50
  120.0 1.3 %collective-permute-start.51 = (bf16[1,32,256]{2,1,0:T(8,128)(2,1)S(1)}, bf16[1,32,256]{2,1,0:T(8,128)(2,1)S(1)}, u32[]{:S(2)}, u32[]{:S(2)}) collective-permute-start(bf16[1,32,256]{2,1,0:T(8,128)(2,1)S(1)} %collective-permute-done.48), channel_id=1, source_target_pairs={{0,1},{1,0},{2,3},{3,2},{4,5},{5,4},{6,7},{7,6},{8,9},{9,8},{10,11... | collective-permute-start | bytes 49160 | tf_op jit(solution)/shard_map/ppermute | solution.py:271
  (1 other events, 0.8 us)

commit v17 on v16

--- a/solution.py
+++ b/solution.py
@@ -177,9 +177,7 @@
     own_out[...] = keep_ref[0].astype(F32) + swap_ref[0].astype(F32)
     for n, out_ref in enumerate(out_refs):
         total = keep_ref[n + 1].astype(F32) + swap_ref[n + 1].astype(F32)
-        for part_ref in part_refs[n :: len(out_refs)]:
-            total = total + part_ref[...].astype(F32)
-        out_ref[...] = total.astype(BF)
+        out_ref[...] = (total + part_refs[n][...].astype(F32)).astype(BF)
 
 
 def rows_kernel(source_ref, target_ref, source_out, target_out, *, clusters, far, magic, shift):
@@ -371,9 +369,9 @@
         compiler_params=params(16),
     )
     far_add = adder(add_kernel, 2, [part_shape] * 4)
-    middle_add = adder(functools.partial(middle_add_kernel, parts=4), 6, [own_shape] + [part_shape] * 3)
+    middle_add = adder(functools.partial(middle_add_kernel, parts=3), 5, [own_shape] + [part_shape] * 3)
     last_add = adder(
-        functools.partial(last_add_kernel, parts=3), 4, [shape(tile_shape, F32)] + [tile_out] * (far - 1)
+        functools.partial(last_add_kernel, parts=4), 5, [shape(tile_shape, F32)] + [tile_out] * (far - 1)
     )
 
     def finish(with_coeffs):
@@ -404,16 +402,13 @@
         keep_long, keep, send_long, send = totals
         corner, xy, yz, zx = far_add(keep_long, swap_cores(send_long))
         corner, xy, yz, zx, send = barrier((corner, xy, yz, zx, send))
-        to_x, to_y, to_z, corner, swapped = barrier(
-            (swap(xy, y), swap(yz, z), swap(zx, x), swap(corner, y | z), swap_cores(send))
+        to_x, to_y, to_z, swapped = barrier((swap(xy, y), swap(yz, z), swap(zx, x), swap_cores(send)))
+        own, to_x, to_y, to_z, inner, outer = barrier(
+            (*middle_add(keep, swapped, to_x, to_y, to_z), inner, outer)
         )
-        own, to_x, to_y, to_z, inner, outer = barrier(
-            (*middle_add(keep, swapped, to_x, to_y, to_z, corner), inner, outer)
-        )
-        own, to_x, to_y, to_z, inner, outer = barrier(
-            (own, swap(to_x, x), swap(to_y, y), swap(to_z, z), inner, lax.ppermute(outer, "clu", halo_pairs))
-        )
-        total, *away = last_add(own, to_x, to_y, to_z)
+        parts = [swap(to_x, x), swap(to_y, y), swap(to_z, z), swap(corner, x | y | z)]
+        own, parts, inner, outer = barrier((own, parts, inner, lax.ppermute(outer, "clu", halo_pairs)))
+        total, *away = last_add(own, *parts)
         edges = edge(swap_cores(inner), swap_cores(outer), near_field, near_field)
         terms, edges = barrier(([swap_far(part, s + 1) for s, part in enumerate(away)], edges))
         return finish(with_coeffs)(ranks, near_sum, edges, basis, transfer, total, *terms)

time: 127 us -> 126 us (level)
  waiting for transfers between devices: 55.5 us -> 52 us
  starting transfers between devices: 47.8 us -> 50.3 us
    ppermute x4, waiting for transfers between devices: 12.8 us -> 10.5 us  [swap_far(): lax.ppermute(part, 'clu', [(d, (d + shift * cube) % devices) for d in ran...]
  transfers between devices with their start and end apart: 52 -> 52, of which waited for: 37 -> 38; matrix products, arithmetic and copies ran while one was open for 4% -> 4% of each run, Pallas kernels for 2% -> 2%
where the time goes in v17:
time: 126 us
  waiting for transfers between devices  52 us (41%)
  starting transfers between devices  50.3 us (40%)
  Pallas kernels  16.3 us (13%)
  local copies, waits for them, and re-layouts  6.55 us (5%)
    ppermute x28, starting transfers between devices, swap(): lax.ppermute(part, 'clu', [(d, d ^ (turned if d % cores else direction) *...  35.7 us
    ppermute x28, waiting for transfers between devices, swap(): lax.ppermute(part, 'clu', [(d, d ^ (turned if d % cores else direction) *...  25.2 us
    ppermute x4, waiting for transfers between devices, swap_far(): lax.ppermute(part, 'clu', [(d, (d + shift * cube) % devices) for d in ran...  10.5 us
    ppermute x2, waiting for transfers between devices, apply_matrix(): lax.ppermute(outer, 'clu', halo_pairs)  8.64 us
    ppermute x18, waiting for transfers between devices, swap_cores(): return lax.ppermute(part, 'clu', [(d, d ^ 1) for d in range(devices)])  7.58 us
    ppermute x4, starting transfers between devices, swap_far(): lax.ppermute(part, 'clu', [(d, (d + shift * cube) % devices) for d in ran...  7.51 us
    pallas_call x2, Pallas kernels, apply_matrix(): couple(source_rows, target_rows, coupling, near_pieces, *far_pieces, othe...  7.21 us
    unnamed x27, local copies, waits for them, and re-layouts  6.55 us
  transfers between devices with their start and end apart: 52, of which 38 were waited for; matrix products, arithmetic and copies ran while one was open for 4% of the time, Pallas kernels for 2%

profile of v17, /device:TPU:0, one launch (start us, length us, event | category | flops | bytes accessed | tf_op | source)
XLA Modules:
  0.0 126.0 jit_solution(17377007301747892315)
XLA Ops:
  0.6 2.9 %shard_map.95 = (bf16[9,32,128]{2,1,0:T(8,128)(2,1)}, bf16[1,32,256]{2,1,0:T(8,128)(2,1)}, bf16[1,32,256]{2,1,0:T(8,128)(2,1)}) custom-call(s32[12]{0:T(128)} %ranks_ref.5, bf16[8,32,256]{2,1,0:T(8,128)(2,1)} %v_ref.1, bf16[8,96,256]{2,1,0:T(8,128)(2,1)} %basis_ref.3, bf16[8,96,96]{2,1,0:T(8,128)(2,1)} %transfer_ref.3), custom_call_target="tpu_custom_call" | custom-call | tf_op jit(solution)/shard_map/pallas_call | solution.py:292
  3.6 4.1 %collective-permute-start = (bf16[9,32,128]{2,1,0:T(8,128)(2,1)}, bf16[9,32,128]{2,1,0:T(8,128)(2,1)S(1)}, u32[]{:S(2)}, u32[]{:S(2)}) collective-permute-start(bf16[9,32,128]{2,1,0:T(8,128)(2,1)} %get-tuple-element.107.__.refs_0_), channel_id=1, source_target_pairs={{0,16},{1,17},{2,18},{3,19},{4,20},{5,21},{6,22},{7,23},{8,24},{9,... | collective-permute-start | bytes 221192 | tf_op jit(solution)/shard_map/ppermute | solution.py:260
  7.7 4.8 %copy.10._.coupling_ref = bf16[128,96,96]{2,1,0:T(8,128)(2,1)} copy(bf16[128,96,96]{0,2,1:T(8,128)(2,1)} %param.12) | data formatting | bytes 4718592 | tf_op args[4]
  12.4 0.6 shard_map.96._
  13.0 0.8 copy-done.7
  13.9 1.6 %collective-permute-start.3 = (bf16[2,9,32,128]{3,2,1,0:T(8,128)(2,1)S(1)}, bf16[2,9,32,128]{3,2,1,0:T(8,128)(2,1)S(1)}, u32[]{:S(2)}, u32[]{:S(2)}) collective-permute-start(bf16[2,9,32,128]{3,2,1,0:T(8,128)(2,1)S(1)} %shard_map.97.refs_0_), channel_id=1, source_target_pairs={{0,8},{1,3},{2,10},{3,1},{4,12},{5,7},{6,14},{7,5},{8,0},{9,11},{1... | collective-permute-start | bytes 442376 | tf_op jit(solution)/shard_map/ppermute | solution.py:264
  15.5 1.5 %collective-permute-start.2 = (bf16[2,9,32,128]{3,2,1,0:T(8,128)(2,1)S(1)}, bf16[2,9,32,128]{3,2,1,0:T(8,128)(2,1)S(1)}, u32[]{:S(2)}, u32[]{:S(2)}) collective-permute-start(bf16[2,9,32,128]{3,2,1,0:T(8,128)(2,1)S(1)} %shard_map.97.refs_0_), channel_id=1, source_target_pairs={{0,4},{1,9},{2,6},{3,11},{4,0},{5,13},{6,2},{7,15},{8,12},{9,1},{1... | collective-permute-start | bytes 442376 | tf_op jit(solution)/shard_map/ppermute | solution.py:264
  17.0 1.5 %collective-permute-start.1 = (bf16[2,9,32,128]{3,2,1,0:T(8,128)(2,1)S(1)}, bf16[2,9,32,128]{3,2,1,0:T(8,128)(2,1)S(1)}, u32[]{:S(2)}, u32[]{:S(2)}) collective-permute-start(bf16[2,9,32,128]{3,2,1,0:T(8,128)(2,1)S(1)} %shard_map.97.refs_0_), channel_id=1, source_target_pairs={{0,2},{1,5},{2,0},{3,7},{4,6},{5,1},{6,4},{7,3},{8,10},{9,13},{10,... | collective-permute-start | bytes 442376 | tf_op jit(solution)/shard_map/ppermute | solution.py:264
  18.5 0.6 shard_map.98.near_ref
  19.1 1.3 %collective-permute-done.3.refs_3_ = bf16[2,9,32,128]{3,2,1,0:T(8,128)(2,1)S(1)} collective-permute-done((bf16[2,9,32,128]{3,2,1,0:T(8,128)(2,1)S(1)}, bf16[2,9,32,128]{3,2,1,0:T(8,128)(2,1)S(1)}, u32[]{:S(2)}, u32[]{:S(2)}) %collective-permute-start.3) | collective-permute-done | bytes 147488 | tf_op jit(solution)/shard_map/ppermute | solution.py:264
  20.5 1.3 %collective-permute-done.2.refs_2_ = bf16[2,9,32,128]{3,2,1,0:T(8,128)(2,1)S(1)} collective-permute-done((bf16[2,9,32,128]{3,2,1,0:T(8,128)(2,1)S(1)}, bf16[2,9,32,128]{3,2,1,0:T(8,128)(2,1)S(1)}, u32[]{:S(2)}, u32[]{:S(2)}) %collective-permute-start.2) | collective-permute-done | bytes 147488 | tf_op jit(solution)/shard_map/ppermute | solution.py:264
  22.3 0.5 collective-permute-start.6
  22.8 1.5 %collective-permute-start.7 = (bf16[2,9,32,128]{3,2,1,0:T(8,128)(2,1)S(1)}, bf16[2,9,32,128]{3,2,1,0:T(8,128)(2,1)S(1)}, u32[]{:S(2)}, u32[]{:S(2)}) collective-permute-start(bf16[2,9,32,128]{3,2,1,0:T(8,128)(2,1)S(1)} %collective-permute-done.3.refs_3_), channel_id=1, source_target_pairs={{0,2},{1,5},{2,0},{3,7},{4,6},{5,1},{6,4},{7,3},{8,10},{9,13},{10,... | collective-permute-start | bytes 442376 | tf_op jit(solution)/shard_map/ppermute | solution.py:264
  24.3 0.5 collective-permute-start.5
  24.8 2.5 %collective-permute-start.4 = (bf16[2,9,32,128]{3,2,1,0:T(8,128)(2,1)S(1)}, bf16[2,9,32,128]{3,2,1,0:T(8,128)(2,1)S(1)}, u32[]{:S(2)}, u32[]{:S(2)}) collective-permute-start(bf16[2,9,32,128]{3,2,1,0:T(8,128)(2,1)S(1)} %collective-permute-done.1.refs_1_), channel_id=1, source_target_pairs={{0,12},{1,11},{2,14},{3,9},{4,8},{5,15},{6,10},{7,13},{8,4},{9,3},... | collective-permute-start | bytes 442376 | tf_op jit(solution)/shard_map/ppermute | solution.py:264
  27.4 0.9 collective-permute-done.6.refs_3_
  28.6 1.6 %collective-permute-done.5.refs_2_ = bf16[2,9,32,128]{3,2,1,0:T(8,128)(2,1)S(1)} collective-permute-done((bf16[2,9,32,128]{3,2,1,0:T(8,128)(2,1)S(1)}, bf16[2,9,32,128]{3,2,1,0:T(8,128)(2,1)S(1)}, u32[]{:S(2)}, u32[]{:S(2)}) %collective-permute-start.5) | collective-permute-done | bytes 147488 | tf_op jit(solution)/shard_map/ppermute | solution.py:264
  30.2 2.3 %collective-permute-done.4.refs_1_ = bf16[2,9,32,128]{3,2,1,0:T(8,128)(2,1)S(1)} collective-permute-done((bf16[2,9,32,128]{3,2,1,0:T(8,128)(2,1)S(1)}, bf16[2,9,32,128]{3,2,1,0:T(8,128)(2,1)S(1)}, u32[]{:S(2)}, u32[]{:S(2)}) %collective-permute-start.4) | collective-permute-done | bytes 147488 | tf_op jit(solution)/shard_map/ppermute | solution.py:264
  34.9 3.6 %shard_map.101 = (bf16[4,2,9,32,128]{4,3,2,1,0:T(8,128)(2,1)S(1)}, bf16[4,2,9,32,128]{4,3,2,1,0:T(8,128)(2,1)S(1)}, bf16[4,2,9,32,128]{4,3,2,1,0:T(8,128)(2,1)S(1)}, bf16[4,2,9,32,128]{4,3,2,1,0:T(8,128)(2,1)S(1)}) custom-call(s32[128]{0:T(128)S(1)} %bitcast.4, s32[128]{0:T(128)S(1)} %bitcast.6, bf16[128,96,96]{2,1,0:T(8,128)(2,1)S(1)} %copy-done.1, ...), custom_call_target="tpu_custom_call" | custom-call | flops 75497472 | bytes 10485760 | tf_op jit(solution)/shard_map/pallas_call | solution.py:401
  38.8 1.8 %collective-permute-done.13.swap_ref = bf16[4,2,9,32,128]{4,3,2,1,0:T(8,128)(2,1)S(1)} collective-permute-done((bf16[4,2,9,32,128]{4,3,2,1,0:T(8,128)(2,1)S(1)}, bf16[4,2,9,32,128]{4,3,2,1,0:T(8,128)(2,1)S(1)}, u32[]{:S(2)}, u32[]{:S(2)}) %collective-permute-start.13) | collective-permute-done | bytes 589856 | tf_op jit(solution)/shard_map/ppermute | solution.py:269
  41.0 1.0 collective-permute-start.14
  42.5 1.5 %collective-permute-start.16 = (bf16[2,9,32,128]{3,2,1,0:T(8,128)(2,1)S(1)}, bf16[2,9,32,128]{3,2,1,0:T(8,128)(2,1)S(1)}, u32[]{:S(2)}, u32[]{:S(2)}) collective-permute-start(bf16[2,9,32,128]{3,2,1,0:T(8,128)(2,1)S(1)} %get-tuple-element.130), channel_id=1, source_target_pairs={{0,2},{1,5},{2,0},{3,7},{4,6},{5,1},{6,4},{7,3},{8,10},{9,13},{10,... | collective-permute-start | bytes 442376 | tf_op jit(solution)/shard_map/ppermute | solution.py:264
  44.0 2.0 %collective-permute-start.21 = (bf16[2,9,32,128]{3,2,1,0:T(8,128)(2,1)S(1)}, bf16[2,9,32,128]{3,2,1,0:T(8,128)(2,1)S(1)}, u32[]{:S(2)}, u32[]{:S(2)}) collective-permute-start(bf16[2,9,32,128]{3,2,1,0:T(8,128)(2,1)S(1)} %get-tuple-element.146), channel_id=1, source_target_pairs={{0,14},{1,15},{2,12},{3,13},{4,10},{5,11},{6,8},{7,9},{8,6},{9,7},... | collective-permute-start | bytes 442376 | tf_op jit(solution)/shard_map/ppermute | solution.py:264
  46.0 1.6 %collective-permute-done.14.refs_0_ = bf16[2,9,32,128]{3,2,1,0:T(8,128)(2,1)S(1)} collective-permute-done((bf16[2,9,32,128]{3,2,1,0:T(8,128)(2,1)S(1)}, bf16[2,9,32,128]{3,2,1,0:T(8,128)(2,1)S(1)}, u32[]{:S(2)}, u32[]{:S(2)}) %collective-permute-start.14) | collective-permute-done | bytes 147488 | tf_op jit(solution)/shard_map/ppermute | solution.py:264
  47.9 1.9 %collective-permute-done.16.refs_2_ = bf16[2,9,32,128]{3,2,1,0:T(8,128)(2,1)S(1)} collective-permute-done((bf16[2,9,32,128]{3,2,1,0:T(8,128)(2,1)S(1)}, bf16[2,9,32,128]{3,2,1,0:T(8,128)(2,1)S(1)}, u32[]{:S(2)}, u32[]{:S(2)}) %collective-permute-start.16) | collective-permute-done | bytes 147488 | tf_op jit(solution)/shard_map/ppermute | solution.py:264
  50.0 2.5 %collective-permute-start.18 = (bf16[2,9,32,128]{3,2,1,0:T(8,128)(2,1)S(1)}, bf16[2,9,32,128]{3,2,1,0:T(8,128)(2,1)S(1)}, u32[]{:S(2)}, u32[]{:S(2)}) collective-permute-start(bf16[2,9,32,128]{3,2,1,0:T(8,128)(2,1)S(1)} %get-tuple-element.143), channel_id=1, source_target_pairs={{0,2},{1,5},{2,0},{3,7},{4,6},{5,1},{6,4},{7,3},{8,10},{9,13},{10,... | collective-permute-start | bytes 442376 | tf_op jit(solution)/shard_map/ppermute | solution.py:264
  52.5 2.0 %collective-permute-start.20 = (bf16[2,9,32,128]{3,2,1,0:T(8,128)(2,1)S(1)}, bf16[2,9,32,128]{3,2,1,0:T(8,128)(2,1)S(1)}, u32[]{:S(2)}, u32[]{:S(2)}) collective-permute-start(bf16[2,9,32,128]{3,2,1,0:T(8,128)(2,1)S(1)} %get-tuple-element.145), channel_id=1, source_target_pairs={{0,8},{1,3},{2,10},{3,1},{4,12},{5,7},{6,14},{7,5},{8,0},{9,11},{1... | collective-permute-start | bytes 442376 | tf_op jit(solution)/shard_map/ppermute | solution.py:264
  54.6 1.3 %collective-permute-start.22 = (bf16[1,32,256]{2,1,0:T(8,128)(2,1)S(1)}, bf16[1,32,256]{2,1,0:T(8,128)(2,1)S(1)}, u32[]{:S(2)}, u32[]{:S(2)}) collective-permute-start(bf16[1,32,256]{2,1,0:T(8,128)(2,1)S(1)} %copy-done.12), channel_id=1, source_target_pairs={{1,3},{3,5},{5,7},{7,9},{9,11},{11,13},{13,15},{15,17},{17,19},{19... | collective-permute-start | bytes 49160 | tf_op jit(solution)/shard_map/ppermute | solution.py:410
  55.9 4.3 %collective-permute-done.22 = bf16[1,32,256]{2,1,0:T(8,128)(2,1)S(1)} collective-permute-done((bf16[1,32,256]{2,1,0:T(8,128)(2,1)S(1)}, bf16[1,32,256]{2,1,0:T(8,128)(2,1)S(1)}, u32[]{:S(2)}, u32[]{:S(2)}) %collective-permute-start.22) | collective-permute-done | bytes 16416 | tf_op jit(solution)/shard_map/ppermute | solution.py:410
  60.3 1.2 collective-permute-start.23
  61.5 0.5 collective-permute-start.25
  62.0 0.7 collective-permute-done.24.inner_ref
  63.0 3.4 %collective-permute-done.23.rest_0_ = bf16[9,32,128]{2,1,0:T(8,128)(2,1)S(1)} collective-permute-done((bf16[9,32,128]{2,1,0:T(8,128)(2,1)S(1)}, bf16[9,32,128]{2,1,0:T(8,128)(2,1)S(1)}, u32[]{:S(2)}, u32[]{:S(2)}) %collective-permute-start.23) | collective-permute-done | bytes 73760 | tf_op jit(solution)/shard_map/ppermute | solution.py:260
  66.4 1.6 %shard_map.106 = (bf16[8,32,256]{2,1,0:T(8,128)(2,1)}, bf16[9,32,128]{2,1,0:T(8,128)(2,1)S(1)}, bf16[1,32,256]{2,1,0:T(8,128)(2,1)S(1)}, bf16[1,32,256]{2,1,0:T(8,128)(2,1)S(1)}) custom-call(s32[12]{0:T(128)S(1)} %copy-done.8, f32[8,32,256]{2,1,0:T(8,128)S(1)} %shard_map.98.near_ref, f32[2,32,256]{2,1,0:T(8,128)S(1)} %shard_map.105.edge_ref, ...), custom_call_target="tpu_custom_call" | custom-call | tf_op jit(solution)/shard_map/pallas_call | solution.py:414
  68.5 5.1 %collective-permute-done.26.refs_1_ = bf16[9,32,128]{2,1,0:T(8,128)(2,1)S(1)} collective-permute-done((bf16[9,32,128]{2,1,0:T(8,128)(2,1)S(1)}, bf16[9,32,128]{2,1,0:T(8,128)(2,1)S(1)}, u32[]{:S(2)}, u32[]{:S(2)}) %collective-permute-start.26) | collective-permute-done | bytes 73760 | tf_op jit(solution)/shard_map/ppermute | solution.py:260
  73.6 1.4 %collective-permute-start.28 = (bf16[2,9,32,128]{3,2,1,0:T(8,128)(2,1)S(1)}, bf16[2,9,32,128]{3,2,1,0:T(8,128)(2,1)S(1)}, u32[]{:S(2)}, u32[]{:S(2)}) collective-permute-start(bf16[2,9,32,128]{3,2,1,0:T(8,128)(2,1)S(1)} %shard_map.107.refs_0_), channel_id=1, source_target_pairs={{0,4},{1,9},{2,6},{3,11},{4,0},{5,13},{6,2},{7,15},{8,12},{9,1},{1... | collective-permute-start | bytes 442376 | tf_op jit(solution)/shard_map/ppermute | solution.py:264
  75.0 1.9 %collective-permute-start.27 = (bf16[2,9,32,128]{3,2,1,0:T(8,128)(2,1)S(1)}, bf16[2,9,32,128]{3,2,1,0:T(8,128)(2,1)S(1)}, u32[]{:S(2)}, u32[]{:S(2)}) collective-permute-start(bf16[2,9,32,128]{3,2,1,0:T(8,128)(2,1)S(1)} %shard_map.107.refs_0_), channel_id=1, source_target_pairs={{0,2},{1,5},{2,0},{3,7},{4,6},{5,1},{6,4},{7,3},{8,10},{9,13},{10,... | collective-permute-start | bytes 442376 | tf_op jit(solution)/shard_map/ppermute | solution.py:264
  76.9 0.9 copy-done.6
  77.8 0.6 shard_map.108.near_ref
  78.8 1.3 %collective-permute-done.27.refs_1_ = bf16[2,9,32,128]{3,2,1,0:T(8,128)(2,1)S(1)} collective-permute-done((bf16[2,9,32,128]{3,2,1,0:T(8,128)(2,1)S(1)}, bf16[2,9,32,128]{3,2,1,0:T(8,128)(2,1)S(1)}, u32[]{:S(2)}, u32[]{:S(2)}) %collective-permute-start.27) | collective-permute-done | bytes 147488 | tf_op jit(solution)/shard_map/ppermute | solution.py:264
  80.3 2.0 %collective-permute-start.32 = (bf16[2,9,32,128]{3,2,1,0:T(8,128)(2,1)S(1)}, bf16[2,9,32,128]{3,2,1,0:T(8,128)(2,1)S(1)}, u32[]{:S(2)}, u32[]{:S(2)}) collective-permute-start(bf16[2,9,32,128]{3,2,1,0:T(8,128)(2,1)S(1)} %collective-permute-done.28.refs_2_), channel_id=1, source_target_pairs={{0,8},{1,3},{2,10},{3,1},{4,12},{5,7},{6,14},{7,5},{8,0},{9,11},{1... | collective-permute-start | bytes 442376 | tf_op jit(solution)/shard_map/ppermute | solution.py:264
  82.3 1.9 %collective-permute-start.33 = (bf16[2,9,32,128]{3,2,1,0:T(8,128)(2,1)S(1)}, bf16[2,9,32,128]{3,2,1,0:T(8,128)(2,1)S(1)}, u32[]{:S(2)}, u32[]{:S(2)}) collective-permute-start(bf16[2,9,32,128]{3,2,1,0:T(8,128)(2,1)S(1)} %collective-permute-done.29.refs_3_), channel_id=1, source_target_pairs={{0,2},{1,5},{2,0},{3,7},{4,6},{5,1},{6,4},{7,3},{8,10},{9,13},{10,... | collective-permute-start | bytes 442376 | tf_op jit(solution)/shard_map/ppermute | solution.py:264
  84.2 0.7 collective-permute-start.31
  84.9 0.8 collective-permute-start.30
  85.7 2.7 %collective-permute-done.33.refs_4_ = bf16[2,9,32,128]{3,2,1,0:T(8,128)(2,1)S(1)} collective-permute-done((bf16[2,9,32,128]{3,2,1,0:T(8,128)(2,1)S(1)}, bf16[2,9,32,128]{3,2,1,0:T(8,128)(2,1)S(1)}, u32[]{:S(2)}, u32[]{:S(2)}) %collective-permute-start.33) | collective-permute-done | bytes 147488 | tf_op jit(solution)/shard_map/ppermute | solution.py:264
  88.4 0.9 collective-permute-done.31.refs_2_
  89.3 1.8 %collective-permute-done.30.refs_1_ = bf16[2,9,32,128]{3,2,1,0:T(8,128)(2,1)S(1)} collective-permute-done((bf16[2,9,32,128]{3,2,1,0:T(8,128)(2,1)S(1)}, bf16[2,9,32,128]{3,2,1,0:T(8,128)(2,1)S(1)}, u32[]{:S(2)}, u32[]{:S(2)}) %collective-permute-start.30) | collective-permute-done | bytes 147488 | tf_op jit(solution)/shard_map/ppermute | solution.py:264
  93.2 3.6 %shard_map.110 = (bf16[4,2,9,32,128]{4,3,2,1,0:T(8,128)(2,1)S(1)}, bf16[4,2,9,32,128]{4,3,2,1,0:T(8,128)(2,1)S(1)}, bf16[4,2,9,32,128]{4,3,2,1,0:T(8,128)(2,1)S(1)}, bf16[4,2,9,32,128]{4,3,2,1,0:T(8,128)(2,1)S(1)}) custom-call(s32[128]{0:T(128)S(1)} %bitcast.5, s32[128]{0:T(128)S(1)} %bitcast.7, bf16[128,96,96]{2,1,0:T(8,128)(2,1)S(1)} %copy-done.1, ...), custom_call_target="tpu_custom_call" | custom-call | flops 75497472 | bytes 10485760 | tf_op jit(solution)/shard_map/pallas_call | solution.py:401
  97.2 1.7 %collective-permute-done.39.swap_ref = bf16[4,2,9,32,128]{4,3,2,1,0:T(8,128)(2,1)S(1)} collective-permute-done((bf16[4,2,9,32,128]{4,3,2,1,0:T(8,128)(2,1)S(1)}, bf16[4,2,9,32,128]{4,3,2,1,0:T(8,128)(2,1)S(1)}, u32[]{:S(2)}, u32[]{:S(2)}) %collective-permute-start.39) | collective-permute-done | bytes 589856 | tf_op jit(solution)/shard_map/ppermute | solution.py:269
  99.4 1.1 collective-permute-start.40
  100.5 1.5 %collective-permute-start.41 = (bf16[2,9,32,128]{3,2,1,0:T(8,128)(2,1)S(1)}, bf16[2,9,32,128]{3,2,1,0:T(8,128)(2,1)S(1)}, u32[]{:S(2)}, u32[]{:S(2)}) collective-permute-start(bf16[2,9,32,128]{3,2,1,0:T(8,128)(2,1)S(1)} %get-tuple-element.181), channel_id=1, source_target_pairs={{0,8},{1,3},{2,10},{3,1},{4,12},{5,7},{6,14},{7,5},{8,0},{9,11},{1... | collective-permute-start | bytes 442376 | tf_op jit(solution)/shard_map/ppermute | solution.py:264
  102.0 1.7 %collective-permute-start.42 = (bf16[2,9,32,128]{3,2,1,0:T(8,128)(2,1)S(1)}, bf16[2,9,32,128]{3,2,1,0:T(8,128)(2,1)S(1)}, u32[]{:S(2)}, u32[]{:S(2)}) collective-permute-start(bf16[2,9,32,128]{3,2,1,0:T(8,128)(2,1)S(1)} %get-tuple-element.182), channel_id=1, source_target_pairs={{0,2},{1,5},{2,0},{3,7},{4,6},{5,1},{6,4},{7,3},{8,10},{9,13},{10,... | collective-permute-start | bytes 442376 | tf_op jit(solution)/shard_map/ppermute | solution.py:264
  103.7 0.6 collective-permute-start.47
  104.7 1.0 collective-permute-done.41.refs_1_
  105.7 4.7 %collective-permute-done.42.refs_2_ = bf16[2,9,32,128]{3,2,1,0:T(8,128)(2,1)S(1)} collective-permute-done((bf16[2,9,32,128]{3,2,1,0:T(8,128)(2,1)S(1)}, bf16[2,9,32,128]{3,2,1,0:T(8,128)(2,1)S(1)}, u32[]{:S(2)}, u32[]{:S(2)}) %collective-permute-start.42) | collective-permute-done | bytes 147488 | tf_op jit(solution)/shard_map/ppermute | solution.py:264
  110.5 1.8 %collective-permute-start.44 = (bf16[2,9,32,128]{3,2,1,0:T(8,128)(2,1)S(1)}, bf16[2,9,32,128]{3,2,1,0:T(8,128)(2,1)S(1)}, u32[]{:S(2)}, u32[]{:S(2)}) collective-permute-start(bf16[2,9,32,128]{3,2,1,0:T(8,128)(2,1)S(1)} %get-tuple-element.195), channel_id=1, source_target_pairs={{0,2},{1,5},{2,0},{3,7},{4,6},{5,1},{6,4},{7,3},{8,10},{9,13},{10,... | collective-permute-start | bytes 442376 | tf_op jit(solution)/shard_map/ppermute | solution.py:264
  112.3 0.5 collective-permute-start.45
  113.3 1.3 %collective-permute-start.48 = (bf16[1,32,256]{2,1,0:T(8,128)(2,1)S(1)}, bf16[1,32,256]{2,1,0:T(8,128)(2,1)S(1)}, u32[]{:S(2)}, u32[]{:S(2)}) collective-permute-start(bf16[1,32,256]{2,1,0:T(8,128)(2,1)S(1)} %get-tuple-element.200), channel_id=1, source_target_pairs={{1,3},{3,5},{5,7},{7,9},{9,11},{11,13},{13,15},{15,17},{17,19},{19... | collective-permute-start | bytes 49160 | tf_op jit(solution)/shard_map/ppermute | solution.py:410
  114.6 4.3 %collective-permute-done.48 = bf16[1,32,256]{2,1,0:T(8,128)(2,1)S(1)} collective-permute-done((bf16[1,32,256]{2,1,0:T(8,128)(2,1)S(1)}, bf16[1,32,256]{2,1,0:T(8,128)(2,1)S(1)}, u32[]{:S(2)}, u32[]{:S(2)}) %collective-permute-start.48) | collective-permute-done | bytes 16416 | tf_op jit(solution)/shard_map/ppermute | solution.py:410
  119.1 1.8 %collective-permute-start.49 = (bf16[9,32,128]{2,1,0:T(8,128)(2,1)S(1)}, bf16[9,32,128]{2,1,0:T(8,128)(2,1)S(1)}, u32[]{:S(2)}, u32[]{:S(2)}) collective-permute-start(bf16[9,32,128]{2,1,0:T(8,128)(2,1)S(1)} %get-tuple-element.206), channel_id=1, source_target_pairs={{0,16},{1,17},{2,18},{3,19},{4,20},{5,21},{6,22},{7,23},{8,24},{9,... | collective-permute-start | bytes 221192 | tf_op jit(solution)/shard_map/ppermute | solution.py:260
  120.9 0.5 collective-permute-start.51
  121.4 0.7 collective-permute-done.50.inner_ref
  122.3 2.0 %collective-permute-done.49.rest_0_ = bf16[9,32,128]{2,1,0:T(8,128)(2,1)S(1)} collective-permute-done((bf16[9,32,128]{2,1,0:T(8,128)(2,1)S(1)}, bf16[9,32,128]{2,1,0:T(8,128)(2,1)S(1)}, u32[]{:S(2)}, u32[]{:S(2)}) %collective-permute-start.49) | collective-permute-done | bytes 73760 | tf_op jit(solution)/shard_map/ppermute | solution.py:260
  124.4 1.6 %shard_map.115 = bf16[8,32,256]{2,1,0:T(8,128)(2,1)} custom-call(s32[12]{0:T(128)S(1)} %copy-done.8, f32[8,32,256]{2,1,0:T(8,128)S(1)} %shard_map.108.near_ref, f32[2,32,256]{2,1,0:T(8,128)S(1)} %shard_map.114.edge_ref, bf16[8,96,256]{2,1,0:T(8,128)(2,1)S(1)} %copy-done.2, bf16[8,96,96]{2,1,0:T(8,128)(2,1)S(1)} %copy-done.3, ...), custom_call_target="tpu_custom_call" | custom-call | tf_op jit(solution)/shard_map/pallas_call | solution.py:414
  (88 shorter events, 10.9 us)
Async XLA Ops:
  3.5 9.5 %copy-start.5 = (bf16[9,32,128]{2,1,0:T(8,128)(2,1)S(1)}, bf16[9,32,128]{2,1,0:T(8,128)(2,1)}, u32[]{:S(2)}) copy-start(bf16[9,32,128]{2,1,0:T(8,128)(2,1)} %get-tuple-element.107.__.refs_0_) | copy-start | bytes 221188
  3.5 15.0 %copy-start = (bf16[8,3,256,256]{3,2,1,0:T(8,128)(2,1)S(1)}, bf16[8,3,256,256]{3,2,1,0:T(8,128)(2,1)}, u32[]{:S(2)}) copy-start(bf16[8,3,256,256]{3,2,1,0:T(8,128)(2,1)} %last_ref.3) | copy-start | bytes 9437188
  3.6 15.0 %copy-start.4 = (bf16[8,32,256]{2,1,0:T(8,128)(2,1)S(1)}, bf16[8,32,256]{2,1,0:T(8,128)(2,1)}, u32[]{:S(2)}) copy-start(bf16[8,32,256]{2,1,0:T(8,128)(2,1)} %v_ref.1) | copy-start | bytes 393220
  3.6 9.5 %collective-permute-start = (bf16[9,32,128]{2,1,0:T(8,128)(2,1)}, bf16[9,32,128]{2,1,0:T(8,128)(2,1)S(1)}, u32[]{:S(2)}, u32[]{:S(2)}) collective-permute-start(bf16[9,32,128]{2,1,0:T(8,128)(2,1)} %get-tuple-element.107.__.refs_0_), channel_id=1, source_target_pairs={{0,16},{1,17},{2,18},{3,19},{4,20},{5,21},{6,22},{7,23},{8,24},{9,... | collective-permute-start | bytes 221192 | tf_op jit(solution)/shard_map/ppermute | solution.py:260
  13.0 21.9 %copy-start.1 = (bf16[128,96,96]{2,1,0:T(8,128)(2,1)S(1)}, bf16[128,96,96]{2,1,0:T(8,128)(2,1)}, u32[]{:S(2)}) copy-start(bf16[128,96,96]{2,1,0:T(8,128)(2,1)} %copy.10._.coupling_ref) | copy-start | bytes 7077892
  13.9 19.7 %copy-start.9 = (s32[128]{0:T(128)S(1)}, s32[128]{0:T(128)}, u32[]{:S(2)}) copy-start(s32[128]{0:T(128)} %param.14) | copy-start | bytes 1540
  13.9 19.7 %copy-start.10 = (s32[128]{0:T(128)S(1)}, s32[128]{0:T(128)}, u32[]{:S(2)}) copy-start(s32[128]{0:T(128)} %param.15) | copy-start | bytes 1540
  13.9 6.6 %collective-permute-start.3 = (bf16[2,9,32,128]{3,2,1,0:T(8,128)(2,1)S(1)}, bf16[2,9,32,128]{3,2,1,0:T(8,128)(2,1)S(1)}, u32[]{:S(2)}, u32[]{:S(2)}) collective-permute-start(bf16[2,9,32,128]{3,2,1,0:T(8,128)(2,1)S(1)} %shard_map.97.refs_0_), channel_id=1, source_target_pairs={{0,8},{1,3},{2,10},{3,1},{4,12},{5,7},{6,14},{7,5},{8,0},{9,11},{1... | collective-permute-start | bytes 442376 | tf_op jit(solution)/shard_map/ppermute | solution.py:264
  15.5 6.2 %collective-permute-start.2 = (bf16[2,9,32,128]{3,2,1,0:T(8,128)(2,1)S(1)}, bf16[2,9,32,128]{3,2,1,0:T(8,128)(2,1)S(1)}, u32[]{:S(2)}, u32[]{:S(2)}) collective-permute-start(bf16[2,9,32,128]{3,2,1,0:T(8,128)(2,1)S(1)} %shard_map.97.refs_0_), channel_id=1, source_target_pairs={{0,4},{1,9},{2,6},{3,11},{4,0},{5,13},{6,2},{7,15},{8,12},{9,1},{1... | collective-permute-start | bytes 442376 | tf_op jit(solution)/shard_map/ppermute | solution.py:264
  17.0 5.1 %collective-permute-start.1 = (bf16[2,9,32,128]{3,2,1,0:T(8,128)(2,1)S(1)}, bf16[2,9,32,128]{3,2,1,0:T(8,128)(2,1)S(1)}, u32[]{:S(2)}, u32[]{:S(2)}) collective-permute-start(bf16[2,9,32,128]{3,2,1,0:T(8,128)(2,1)S(1)} %shard_map.97.refs_0_), channel_id=1, source_target_pairs={{0,2},{1,5},{2,0},{3,7},{4,6},{5,1},{6,4},{7,3},{8,10},{9,13},{10,... | collective-permute-start | bytes 442376 | tf_op jit(solution)/shard_map/ppermute | solution.py:264
  22.2 10.3 %collective-permute-start.8 = (bf16[4,2,9,32,128]{4,3,2,1,0:T(8,128)(2,1)S(1)}, bf16[4,2,9,32,128]{4,3,2,1,0:T(8,128)(2,1)S(1)}, u32[]{:S(2)}, u32[]{:S(2)}) collective-permute-start(bf16[4,2,9,32,128]{4,3,2,1,0:T(8,128)(2,1)S(1)} %shard_map.100.refs_0_), channel_id=1, source_target_pairs={{0,1},{1,0},{2,3},{3,2},{4,5},{5,4},{6,7},{7,6},{8,9},{9,8},{10,11... | collective-permute-start | bytes 1769480 | tf_op jit(solution)/shard_map/ppermute | solution.py:269
  22.3 5.9 %collective-permute-start.6 = (bf16[2,9,32,128]{3,2,1,0:T(8,128)(2,1)S(1)}, bf16[2,9,32,128]{3,2,1,0:T(8,128)(2,1)S(1)}, u32[]{:S(2)}, u32[]{:S(2)}) collective-permute-start(bf16[2,9,32,128]{3,2,1,0:T(8,128)(2,1)S(1)} %collective-permute-done.2.refs_2_), channel_id=1, source_target_pairs={{0,8},{1,3},{2,10},{3,1},{4,12},{5,7},{6,14},{7,5},{8,0},{9,11},{1... | collective-permute-start | bytes 442376 | tf_op jit(solution)/shard_map/ppermute | solution.py:264
  22.8 5.7 %collective-permute-start.7 = (bf16[2,9,32,128]{3,2,1,0:T(8,128)(2,1)S(1)}, bf16[2,9,32,128]{3,2,1,0:T(8,128)(2,1)S(1)}, u32[]{:S(2)}, u32[]{:S(2)}) collective-permute-start(bf16[2,9,32,128]{3,2,1,0:T(8,128)(2,1)S(1)} %collective-permute-done.3.refs_3_), channel_id=1, source_target_pairs={{0,2},{1,5},{2,0},{3,7},{4,6},{5,1},{6,4},{7,3},{8,10},{9,13},{10,... | collective-permute-start | bytes 442376 | tf_op jit(solution)/shard_map/ppermute | solution.py:264
  24.3 5.9 %collective-permute-start.5 = (bf16[2,9,32,128]{3,2,1,0:T(8,128)(2,1)S(1)}, bf16[2,9,32,128]{3,2,1,0:T(8,128)(2,1)S(1)}, u32[]{:S(2)}, u32[]{:S(2)}) collective-permute-start(bf16[2,9,32,128]{3,2,1,0:T(8,128)(2,1)S(1)} %collective-permute-done.1.refs_1_), channel_id=1, source_target_pairs={{0,4},{1,9},{2,6},{3,11},{4,0},{5,13},{6,2},{7,15},{8,12},{9,1},{1... | collective-permute-start | bytes 442376 | tf_op jit(solution)/shard_map/ppermute | solution.py:264
  24.8 7.7 %collective-permute-start.4 = (bf16[2,9,32,128]{3,2,1,0:T(8,128)(2,1)S(1)}, bf16[2,9,32,128]{3,2,1,0:T(8,128)(2,1)S(1)}, u32[]{:S(2)}, u32[]{:S(2)}) collective-permute-start(bf16[2,9,32,128]{3,2,1,0:T(8,128)(2,1)S(1)} %collective-permute-done.1.refs_1_), channel_id=1, source_target_pairs={{0,12},{1,11},{2,14},{3,9},{4,8},{5,15},{6,10},{7,13},{8,4},{9,3},... | collective-permute-start | bytes 442376 | tf_op jit(solution)/shard_map/ppermute | solution.py:264
  32.5 1.5 %collective-permute-start.9 = (bf16[2,9,32,128]{3,2,1,0:T(8,128)(2,1)S(1)}, bf16[2,9,32,128]{3,2,1,0:T(8,128)(2,1)S(1)}, u32[]{:S(2)}, u32[]{:S(2)}) collective-permute-start(bf16[2,9,32,128]{3,2,1,0:T(8,128)(2,1)S(1)} %collective-permute-done.4.refs_1_), channel_id=1, source_target_pairs={{0,1},{1,0},{2,3},{3,2},{4,5},{5,4},{6,7},{7,6},{8,9},{9,8},{10,11... | collective-permute-start | bytes 442376 | tf_op jit(solution)/shard_map/ppermute | solution.py:269
  33.0 1.4 %collective-permute-start.10 = (bf16[2,9,32,128]{3,2,1,0:T(8,128)(2,1)S(1)}, bf16[2,9,32,128]{3,2,1,0:T(8,128)(2,1)S(1)}, u32[]{:S(2)}, u32[]{:S(2)}) collective-permute-start(bf16[2,9,32,128]{3,2,1,0:T(8,128)(2,1)S(1)} %collective-permute-done.5.refs_2_), channel_id=1, source_target_pairs={{0,1},{1,0},{2,3},{3,2},{4,5},{5,4},{6,7},{7,6},{8,9},{9,8},{10,11... | collective-permute-start | bytes 442376 | tf_op jit(solution)/shard_map/ppermute | solution.py:269
  33.0 1.6 %collective-permute-start.11 = (bf16[2,9,32,128]{3,2,1,0:T(8,128)(2,1)S(1)}, bf16[2,9,32,128]{3,2,1,0:T(8,128)(2,1)S(1)}, u32[]{:S(2)}, u32[]{:S(2)}) collective-permute-start(bf16[2,9,32,128]{3,2,1,0:T(8,128)(2,1)S(1)} %collective-permute-done.6.refs_3_), channel_id=1, source_target_pairs={{0,1},{1,0},{2,3},{3,2},{4,5},{5,4},{6,7},{7,6},{8,9},{9,8},{10,11... | collective-permute-start | bytes 442376 | tf_op jit(solution)/shard_map/ppermute | solution.py:269
  33.5 1.4 %collective-permute-start.12 = (bf16[2,9,32,128]{3,2,1,0:T(8,128)(2,1)S(1)}, bf16[2,9,32,128]{3,2,1,0:T(8,128)(2,1)S(1)}, u32[]{:S(2)}, u32[]{:S(2)}) collective-permute-start(bf16[2,9,32,128]{3,2,1,0:T(8,128)(2,1)S(1)} %collective-permute-done.7.refs_4_), channel_id=1, source_target_pairs={{0,1},{1,0},{2,3},{3,2},{4,5},{5,4},{6,7},{7,6},{8,9},{9,8},{10,11... | collective-permute-start | bytes 442376 | tf_op jit(solution)/shard_map/ppermute | solution.py:269
  34.9 19.7 %copy-start.12 = (bf16[1,32,256]{2,1,0:T(8,128)(2,1)S(1)}, bf16[1,32,256]{2,1,0:T(8,128)(2,1)}, u32[]{:S(2)}) copy-start(bf16[1,32,256]{2,1,0:T(8,128)(2,1)} %get-tuple-element.148) | copy-start | bytes 49156
  38.5 23.0 %copy-start.11 = (bf16[1,32,256]{2,1,0:T(8,128)(2,1)S(1)}, bf16[1,32,256]{2,1,0:T(8,128)(2,1)}, u32[]{:S(2)}) copy-start(bf16[1,32,256]{2,1,0:T(8,128)(2,1)} %get-tuple-element.155) | copy-start | bytes 49156
  38.5 2.1 %collective-permute-start.13 = (bf16[4,2,9,32,128]{4,3,2,1,0:T(8,128)(2,1)S(1)}, bf16[4,2,9,32,128]{4,3,2,1,0:T(8,128)(2,1)S(1)}, u32[]{:S(2)}, u32[]{:S(2)}) collective-permute-start(bf16[4,2,9,32,128]{4,3,2,1,0:T(8,128)(2,1)S(1)} %get-tuple-element.122), channel_id=1, source_target_pairs={{0,1},{1,0},{2,3},{3,2},{4,5},{5,4},{6,7},{7,6},{8,9},{9,8},{10,11... | collective-permute-start | bytes 1769480 | tf_op jit(solution)/shard_map/ppermute | solution.py:269
  40.7 9.1 %collective-permute-start.17 = (bf16[4,2,9,32,128]{4,3,2,1,0:T(8,128)(2,1)S(1)}, bf16[4,2,9,32,128]{4,3,2,1,0:T(8,128)(2,1)S(1)}, u32[]{:S(2)}, u32[]{:S(2)}) collective-permute-start(bf16[4,2,9,32,128]{4,3,2,1,0:T(8,128)(2,1)S(1)} %get-tuple-element.131), channel_id=1, source_target_pairs={{0,1},{1,0},{2,3},{3,2},{4,5},{5,4},{6,7},{7,6},{8,9},{9,8},{10,11... | collective-permute-start | bytes 1769480 | tf_op jit(solution)/shard_map/ppermute | solution.py:269
  41.0 6.6 %collective-permute-start.14 = (bf16[2,9,32,128]{3,2,1,0:T(8,128)(2,1)S(1)}, bf16[2,9,32,128]{3,2,1,0:T(8,128)(2,1)S(1)}, u32[]{:S(2)}, u32[]{:S(2)}) collective-permute-start(bf16[2,9,32,128]{3,2,1,0:T(8,128)(2,1)S(1)} %get-tuple-element.128), channel_id=1, source_target_pairs={{0,4},{1,9},{2,6},{3,11},{4,0},{5,13},{6,2},{7,15},{8,12},{9,1},{1... | collective-permute-start | bytes 442376 | tf_op jit(solution)/shard_map/ppermute | solution.py:264
  42.0 5.9 %collective-permute-start.15 = (bf16[2,9,32,128]{3,2,1,0:T(8,128)(2,1)S(1)}, bf16[2,9,32,128]{3,2,1,0:T(8,128)(2,1)S(1)}, u32[]{:S(2)}, u32[]{:S(2)}) collective-permute-start(bf16[2,9,32,128]{3,2,1,0:T(8,128)(2,1)S(1)} %get-tuple-element.129), channel_id=1, source_target_pairs={{0,8},{1,3},{2,10},{3,1},{4,12},{5,7},{6,14},{7,5},{8,0},{9,11},{1... | collective-permute-start | bytes 442376 | tf_op jit(solution)/shard_map/ppermute | solution.py:264
  42.5 7.3 %collective-permute-start.16 = (bf16[2,9,32,128]{3,2,1,0:T(8,128)(2,1)S(1)}, bf16[2,9,32,128]{3,2,1,0:T(8,128)(2,1)S(1)}, u32[]{:S(2)}, u32[]{:S(2)}) collective-permute-start(bf16[2,9,32,128]{3,2,1,0:T(8,128)(2,1)S(1)} %get-tuple-element.130), channel_id=1, source_target_pairs={{0,2},{1,5},{2,0},{3,7},{4,6},{5,1},{6,4},{7,3},{8,10},{9,13},{10,... | collective-permute-start | bytes 442376 | tf_op jit(solution)/shard_map/ppermute | solution.py:264
  44.0 11.9 %collective-permute-start.21 = (bf16[2,9,32,128]{3,2,1,0:T(8,128)(2,1)S(1)}, bf16[2,9,32,128]{3,2,1,0:T(8,128)(2,1)S(1)}, u32[]{:S(2)}, u32[]{:S(2)}) collective-permute-start(bf16[2,9,32,128]{3,2,1,0:T(8,128)(2,1)S(1)} %get-tuple-element.146), channel_id=1, source_target_pairs={{0,14},{1,15},{2,12},{3,13},{4,10},{5,11},{6,8},{7,9},{8,6},{9,7},... | collective-permute-start | bytes 442376 | tf_op jit(solution)/shard_map/ppermute | solution.py:264
  50.0 10.2 %collective-permute-start.18 = (bf16[2,9,32,128]{3,2,1,0:T(8,128)(2,1)S(1)}, bf16[2,9,32,128]{3,2,1,0:T(8,128)(2,1)S(1)}, u32[]{:S(2)}, u32[]{:S(2)}) collective-permute-start(bf16[2,9,32,128]{3,2,1,0:T(8,128)(2,1)S(1)} %get-tuple-element.143), channel_id=1, source_target_pairs={{0,2},{1,5},{2,0},{3,7},{4,6},{5,1},{6,4},{7,3},{8,10},{9,13},{10,... | collective-permute-start | bytes 442376 | tf_op jit(solution)/shard_map/ppermute | solution.py:264
  52.5 7.7 %collective-permute-start.19 = (bf16[2,9,32,128]{3,2,1,0:T(8,128)(2,1)S(1)}, bf16[2,9,32,128]{3,2,1,0:T(8,128)(2,1)S(1)}, u32[]{:S(2)}, u32[]{:S(2)}) collective-permute-start(bf16[2,9,32,128]{3,2,1,0:T(8,128)(2,1)S(1)} %get-tuple-element.144), channel_id=1, source_target_pairs={{0,4},{1,9},{2,6},{3,11},{4,0},{5,13},{6,2},{7,15},{8,12},{9,1},{1... | collective-permute-start | bytes 442376 | tf_op jit(solution)/shard_map/ppermute | solution.py:264
  52.5 7.7 %collective-permute-start.20 = (bf16[2,9,32,128]{3,2,1,0:T(8,128)(2,1)S(1)}, bf16[2,9,32,128]{3,2,1,0:T(8,128)(2,1)S(1)}, u32[]{:S(2)}, u32[]{:S(2)}) collective-permute-start(bf16[2,9,32,128]{3,2,1,0:T(8,128)(2,1)S(1)} %get-tuple-element.145), channel_id=1, source_target_pairs={{0,8},{1,3},{2,10},{3,1},{4,12},{5,7},{6,14},{7,5},{8,0},{9,11},{1... | collective-permute-start | bytes 442376 | tf_op jit(solution)/shard_map/ppermute | solution.py:264
  54.6 5.6 %collective-permute-start.22 = (bf16[1,32,256]{2,1,0:T(8,128)(2,1)S(1)}, bf16[1,32,256]{2,1,0:T(8,128)(2,1)S(1)}, u32[]{:S(2)}, u32[]{:S(2)}) collective-permute-start(bf16[1,32,256]{2,1,0:T(8,128)(2,1)S(1)} %copy-done.12), channel_id=1, source_target_pairs={{1,3},{3,5},{5,7},{7,9},{9,11},{11,13},{13,15},{15,17},{17,19},{19... | collective-permute-start | bytes 49160 | tf_op jit(solution)/shard_map/ppermute | solution.py:410
  60.3 6.1 %copy-start.2 = (bf16[8,96,256]{2,1,0:T(8,128)(2,1)S(1)}, bf16[8,96,256]{2,1,0:T(8,128)(2,1)}, u32[]{:S(2)}) copy-start(bf16[8,96,256]{2,1,0:T(8,128)(2,1)} %basis_ref.3) | copy-start | bytes 1179652
  60.3 6.1 %copy-start.3 = (bf16[8,96,96]{2,1,0:T(8,128)(2,1)S(1)}, bf16[8,96,96]{2,1,0:T(8,128)(2,1)}, u32[]{:S(2)}) copy-start(bf16[8,96,96]{2,1,0:T(8,128)(2,1)} %transfer_ref.3) | copy-start | bytes 442372
  60.3 6.1 %copy-start.8 = (s32[12]{0:T(128)S(1)}, s32[12]{0:T(128)}, u32[]{:S(2)}) copy-start(s32[12]{0:T(128)} %ranks_ref.5) | copy-start | bytes 148
  60.3 6.1 %collective-permute-start.23 = (bf16[9,32,128]{2,1,0:T(8,128)(2,1)S(1)}, bf16[9,32,128]{2,1,0:T(8,128)(2,1)S(1)}, u32[]{:S(2)}, u32[]{:S(2)}) collective-permute-start(bf16[9,32,128]{2,1,0:T(8,128)(2,1)S(1)} %get-tuple-element.154), channel_id=1, source_target_pairs={{0,16},{1,17},{2,18},{3,19},{4,20},{5,21},{6,22},{7,23},{8,24},{9,... | collective-permute-start | bytes 221192 | tf_op jit(solution)/shard_map/ppermute | solution.py:260
  61.5 1.2 collective-permute-start.24
  61.5 1.3 %collective-permute-start.25 = (bf16[1,32,256]{2,1,0:T(8,128)(2,1)S(1)}, bf16[1,32,256]{2,1,0:T(8,128)(2,1)S(1)}, u32[]{:S(2)}, u32[]{:S(2)}) collective-permute-start(bf16[1,32,256]{2,1,0:T(8,128)(2,1)S(1)} %collective-permute-done.22), channel_id=1, source_target_pairs={{0,1},{1,0},{2,3},{3,2},{4,5},{5,4},{6,7},{7,6},{8,9},{9,8},{10,11... | collective-permute-start | bytes 49160 | tf_op jit(solution)/shard_map/ppermute | solution.py:269
  68.0 5.5 %collective-permute-start.26 = (bf16[9,32,128]{2,1,0:T(8,128)(2,1)S(1)}, bf16[9,32,128]{2,1,0:T(8,128)(2,1)S(1)}, u32[]{:S(2)}, u32[]{:S(2)}) collective-permute-start(bf16[9,32,128]{2,1,0:T(8,128)(2,1)S(1)} %get-tuple-element.161.refs_0_), channel_id=1, source_target_pairs={{0,16},{1,17},{2,18},{3,19},{4,20},{5,21},{6,22},{7,23},{8,24},{9,... | collective-permute-start | bytes 221192 | tf_op jit(solution)/shard_map/ppermute | solution.py:260
  73.6 5.2 %collective-permute-start.29 = (bf16[2,9,32,128]{3,2,1,0:T(8,128)(2,1)S(1)}, bf16[2,9,32,128]{3,2,1,0:T(8,128)(2,1)S(1)}, u32[]{:S(2)}, u32[]{:S(2)}) collective-permute-start(bf16[2,9,32,128]{3,2,1,0:T(8,128)(2,1)S(1)} %shard_map.107.refs_0_), channel_id=1, source_target_pairs={{0,8},{1,3},{2,10},{3,1},{4,12},{5,7},{6,14},{7,5},{8,0},{9,11},{1... | collective-permute-start | bytes 442376 | tf_op jit(solution)/shard_map/ppermute | solution.py:264
  73.6 5.2 %collective-permute-start.28 = (bf16[2,9,32,128]{3,2,1,0:T(8,128)(2,1)S(1)}, bf16[2,9,32,128]{3,2,1,0:T(8,128)(2,1)S(1)}, u32[]{:S(2)}, u32[]{:S(2)}) collective-permute-start(bf16[2,9,32,128]{3,2,1,0:T(8,128)(2,1)S(1)} %shard_map.107.refs_0_), channel_id=1, source_target_pairs={{0,4},{1,9},{2,6},{3,11},{4,0},{5,13},{6,2},{7,15},{8,12},{9,1},{1... | collective-permute-start | bytes 442376 | tf_op jit(solution)/shard_map/ppermute | solution.py:264
  75.0 5.1 %collective-permute-start.27 = (bf16[2,9,32,128]{3,2,1,0:T(8,128)(2,1)S(1)}, bf16[2,9,32,128]{3,2,1,0:T(8,128)(2,1)S(1)}, u32[]{:S(2)}, u32[]{:S(2)}) collective-permute-start(bf16[2,9,32,128]{3,2,1,0:T(8,128)(2,1)S(1)} %shard_map.107.refs_0_), channel_id=1, source_target_pairs={{0,2},{1,5},{2,0},{3,7},{4,6},{5,1},{6,4},{7,3},{8,10},{9,13},{10,... | collective-permute-start | bytes 442376 | tf_op jit(solution)/shard_map/ppermute | solution.py:264
  76.9 0.9 copy-start.6
  80.2 10.9 %collective-permute-start.34 = (bf16[4,2,9,32,128]{4,3,2,1,0:T(8,128)(2,1)S(1)}, bf16[4,2,9,32,128]{4,3,2,1,0:T(8,128)(2,1)S(1)}, u32[]{:S(2)}, u32[]{:S(2)}) collective-permute-start(bf16[4,2,9,32,128]{4,3,2,1,0:T(8,128)(2,1)S(1)} %shard_map.109.refs_0_), channel_id=1, source_target_pairs={{0,1},{1,0},{2,3},{3,2},{4,5},{5,4},{6,7},{7,6},{8,9},{9,8},{10,11... | collective-permute-start | bytes 1769480 | tf_op jit(solution)/shard_map/ppermute | solution.py:269
  80.3 5.4 %collective-permute-start.32 = (bf16[2,9,32,128]{3,2,1,0:T(8,128)(2,1)S(1)}, bf16[2,9,32,128]{3,2,1,0:T(8,128)(2,1)S(1)}, u32[]{:S(2)}, u32[]{:S(2)}) collective-permute-start(bf16[2,9,32,128]{3,2,1,0:T(8,128)(2,1)S(1)} %collective-permute-done.28.refs_2_), channel_id=1, source_target_pairs={{0,8},{1,3},{2,10},{3,1},{4,12},{5,7},{6,14},{7,5},{8,0},{9,11},{1... | collective-permute-start | bytes 442376 | tf_op jit(solution)/shard_map/ppermute | solution.py:264
  82.3 6.2 %collective-permute-start.33 = (bf16[2,9,32,128]{3,2,1,0:T(8,128)(2,1)S(1)}, bf16[2,9,32,128]{3,2,1,0:T(8,128)(2,1)S(1)}, u32[]{:S(2)}, u32[]{:S(2)}) collective-permute-start(bf16[2,9,32,128]{3,2,1,0:T(8,128)(2,1)S(1)} %collective-permute-done.29.refs_3_), channel_id=1, source_target_pairs={{0,2},{1,5},{2,0},{3,7},{4,6},{5,1},{6,4},{7,3},{8,10},{9,13},{10,... | collective-permute-start | bytes 442376 | tf_op jit(solution)/shard_map/ppermute | solution.py:264
  84.2 5.1 %collective-permute-start.31 = (bf16[2,9,32,128]{3,2,1,0:T(8,128)(2,1)S(1)}, bf16[2,9,32,128]{3,2,1,0:T(8,128)(2,1)S(1)}, u32[]{:S(2)}, u32[]{:S(2)}) collective-permute-start(bf16[2,9,32,128]{3,2,1,0:T(8,128)(2,1)S(1)} %collective-permute-done.27.refs_1_), channel_id=1, source_target_pairs={{0,4},{1,9},{2,6},{3,11},{4,0},{5,13},{6,2},{7,15},{8,12},{9,1},{1... | collective-permute-start | bytes 442376 | tf_op jit(solution)/shard_map/ppermute | solution.py:264
  84.9 6.2 %collective-permute-start.30 = (bf16[2,9,32,128]{3,2,1,0:T(8,128)(2,1)S(1)}, bf16[2,9,32,128]{3,2,1,0:T(8,128)(2,1)S(1)}, u32[]{:S(2)}, u32[]{:S(2)}) collective-permute-start(bf16[2,9,32,128]{3,2,1,0:T(8,128)(2,1)S(1)} %collective-permute-done.27.refs_1_), channel_id=1, source_target_pairs={{0,12},{1,11},{2,14},{3,9},{4,8},{5,15},{6,10},{7,13},{8,4},{9,3},... | collective-permute-start | bytes 442376 | tf_op jit(solution)/shard_map/ppermute | solution.py:264
  91.1 1.4 %collective-permute-start.35 = (bf16[2,9,32,128]{3,2,1,0:T(8,128)(2,1)S(1)}, bf16[2,9,32,128]{3,2,1,0:T(8,128)(2,1)S(1)}, u32[]{:S(2)}, u32[]{:S(2)}) collective-permute-start(bf16[2,9,32,128]{3,2,1,0:T(8,128)(2,1)S(1)} %collective-permute-done.30.refs_1_), channel_id=1, source_target_pairs={{0,1},{1,0},{2,3},{3,2},{4,5},{5,4},{6,7},{7,6},{8,9},{9,8},{10,11... | collective-permute-start | bytes 442376 | tf_op jit(solution)/shard_map/ppermute | solution.py:269
  91.2 1.5 %collective-permute-start.36 = (bf16[2,9,32,128]{3,2,1,0:T(8,128)(2,1)S(1)}, bf16[2,9,32,128]{3,2,1,0:T(8,128)(2,1)S(1)}, u32[]{:S(2)}, u32[]{:S(2)}) collective-permute-start(bf16[2,9,32,128]{3,2,1,0:T(8,128)(2,1)S(1)} %collective-permute-done.31.refs_2_), channel_id=1, source_target_pairs={{0,1},{1,0},{2,3},{3,2},{4,5},{5,4},{6,7},{7,6},{8,9},{9,8},{10,11... | collective-permute-start | bytes 442376 | tf_op jit(solution)/shard_map/ppermute | solution.py:269
  91.6 1.4 %collective-permute-start.37 = (bf16[2,9,32,128]{3,2,1,0:T(8,128)(2,1)S(1)}, bf16[2,9,32,128]{3,2,1,0:T(8,128)(2,1)S(1)}, u32[]{:S(2)}, u32[]{:S(2)}) collective-permute-start(bf16[2,9,32,128]{3,2,1,0:T(8,128)(2,1)S(1)} %collective-permute-done.32.refs_3_), channel_id=1, source_target_pairs={{0,1},{1,0},{2,3},{3,2},{4,5},{5,4},{6,7},{7,6},{8,9},{9,8},{10,11... | collective-permute-start | bytes 442376 | tf_op jit(solution)/shard_map/ppermute | solution.py:269
  91.7 1.5 %collective-permute-start.38 = (bf16[2,9,32,128]{3,2,1,0:T(8,128)(2,1)S(1)}, bf16[2,9,32,128]{3,2,1,0:T(8,128)(2,1)S(1)}, u32[]{:S(2)}, u32[]{:S(2)}) collective-permute-start(bf16[2,9,32,128]{3,2,1,0:T(8,128)(2,1)S(1)} %collective-permute-done.33.refs_4_), channel_id=1, source_target_pairs={{0,1},{1,0},{2,3},{3,2},{4,5},{5,4},{6,7},{7,6},{8,9},{9,8},{10,11... | collective-permute-start | bytes 442376 | tf_op jit(solution)/shard_map/ppermute | solution.py:269
  96.8 2.1 %collective-permute-start.39 = (bf16[4,2,9,32,128]{4,3,2,1,0:T(8,128)(2,1)S(1)}, bf16[4,2,9,32,128]{4,3,2,1,0:T(8,128)(2,1)S(1)}, u32[]{:S(2)}, u32[]{:S(2)}) collective-permute-start(bf16[4,2,9,32,128]{4,3,2,1,0:T(8,128)(2,1)S(1)} %get-tuple-element.174), channel_id=1, source_target_pairs={{0,1},{1,0},{2,3},{3,2},{4,5},{5,4},{6,7},{7,6},{8,9},{9,8},{10,11... | collective-permute-start | bytes 1769480 | tf_op jit(solution)/shard_map/ppermute | solution.py:269
  99.1 11.3 %collective-permute-start.43 = (bf16[4,2,9,32,128]{4,3,2,1,0:T(8,128)(2,1)S(1)}, bf16[4,2,9,32,128]{4,3,2,1,0:T(8,128)(2,1)S(1)}, u32[]{:S(2)}, u32[]{:S(2)}) collective-permute-start(bf16[4,2,9,32,128]{4,3,2,1,0:T(8,128)(2,1)S(1)} %get-tuple-element.183), channel_id=1, source_target_pairs={{0,1},{1,0},{2,3},{3,2},{4,5},{5,4},{6,7},{7,6},{8,9},{9,8},{10,11... | collective-permute-start | bytes 1769480 | tf_op jit(solution)/shard_map/ppermute | solution.py:269
  99.4 5.3 %collective-permute-start.40 = (bf16[2,9,32,128]{3,2,1,0:T(8,128)(2,1)S(1)}, bf16[2,9,32,128]{3,2,1,0:T(8,128)(2,1)S(1)}, u32[]{:S(2)}, u32[]{:S(2)}) collective-permute-start(bf16[2,9,32,128]{3,2,1,0:T(8,128)(2,1)S(1)} %get-tuple-element.180), channel_id=1, source_target_pairs={{0,4},{1,9},{2,6},{3,11},{4,0},{5,13},{6,2},{7,15},{8,12},{9,1},{1... | collective-permute-start | bytes 442376 | tf_op jit(solution)/shard_map/ppermute | solution.py:264
  100.5 5.1 %collective-permute-start.41 = (bf16[2,9,32,128]{3,2,1,0:T(8,128)(2,1)S(1)}, bf16[2,9,32,128]{3,2,1,0:T(8,128)(2,1)S(1)}, u32[]{:S(2)}, u32[]{:S(2)}) collective-permute-start(bf16[2,9,32,128]{3,2,1,0:T(8,128)(2,1)S(1)} %get-tuple-element.181), channel_id=1, source_target_pairs={{0,8},{1,3},{2,10},{3,1},{4,12},{5,7},{6,14},{7,5},{8,0},{9,11},{1... | collective-permute-start | bytes 442376 | tf_op jit(solution)/shard_map/ppermute | solution.py:264
  102.0 8.3 %collective-permute-start.42 = (bf16[2,9,32,128]{3,2,1,0:T(8,128)(2,1)S(1)}, bf16[2,9,32,128]{3,2,1,0:T(8,128)(2,1)S(1)}, u32[]{:S(2)}, u32[]{:S(2)}) collective-permute-start(bf16[2,9,32,128]{3,2,1,0:T(8,128)(2,1)S(1)} %get-tuple-element.182), channel_id=1, source_target_pairs={{0,2},{1,5},{2,0},{3,7},{4,6},{5,1},{6,4},{7,3},{8,10},{9,13},{10,... | collective-permute-start | bytes 442376 | tf_op jit(solution)/shard_map/ppermute | solution.py:264
  103.7 10.9 %collective-permute-start.47 = (bf16[2,9,32,128]{3,2,1,0:T(8,128)(2,1)S(1)}, bf16[2,9,32,128]{3,2,1,0:T(8,128)(2,1)S(1)}, u32[]{:S(2)}, u32[]{:S(2)}) collective-permute-start(bf16[2,9,32,128]{3,2,1,0:T(8,128)(2,1)S(1)} %get-tuple-element.198), channel_id=1, source_target_pairs={{0,14},{1,15},{2,12},{3,13},{4,10},{5,11},{6,8},{7,9},{8,6},{9,7},... | collective-permute-start | bytes 442376 | tf_op jit(solution)/shard_map/ppermute | solution.py:264
  110.5 8.4 %collective-permute-start.44 = (bf16[2,9,32,128]{3,2,1,0:T(8,128)(2,1)S(1)}, bf16[2,9,32,128]{3,2,1,0:T(8,128)(2,1)S(1)}, u32[]{:S(2)}, u32[]{:S(2)}) collective-permute-start(bf16[2,9,32,128]{3,2,1,0:T(8,128)(2,1)S(1)} %get-tuple-element.195), channel_id=1, source_target_pairs={{0,2},{1,5},{2,0},{3,7},{4,6},{5,1},{6,4},{7,3},{8,10},{9,13},{10,... | collective-permute-start | bytes 442376 | tf_op jit(solution)/shard_map/ppermute | solution.py:264
  112.3 6.7 %collective-permute-start.45 = (bf16[2,9,32,128]{3,2,1,0:T(8,128)(2,1)S(1)}, bf16[2,9,32,128]{3,2,1,0:T(8,128)(2,1)S(1)}, u32[]{:S(2)}, u32[]{:S(2)}) collective-permute-start(bf16[2,9,32,128]{3,2,1,0:T(8,128)(2,1)S(1)} %get-tuple-element.196), channel_id=1, source_target_pairs={{0,4},{1,9},{2,6},{3,11},{4,0},{5,13},{6,2},{7,15},{8,12},{9,1},{1... | collective-permute-start | bytes 442376 | tf_op jit(solution)/shard_map/ppermute | solution.py:264
  112.8 6.1 %collective-permute-start.46 = (bf16[2,9,32,128]{3,2,1,0:T(8,128)(2,1)S(1)}, bf16[2,9,32,128]{3,2,1,0:T(8,128)(2,1)S(1)}, u32[]{:S(2)}, u32[]{:S(2)}) collective-permute-start(bf16[2,9,32,128]{3,2,1,0:T(8,128)(2,1)S(1)} %get-tuple-element.197), channel_id=1, source_target_pairs={{0,8},{1,3},{2,10},{3,1},{4,12},{5,7},{6,14},{7,5},{8,0},{9,11},{1... | collective-permute-start | bytes 442376 | tf_op jit(solution)/shard_map/ppermute | solution.py:264
  113.3 5.6 %collective-permute-start.48 = (bf16[1,32,256]{2,1,0:T(8,128)(2,1)S(1)}, bf16[1,32,256]{2,1,0:T(8,128)(2,1)S(1)}, u32[]{:S(2)}, u32[]{:S(2)}) collective-permute-start(bf16[1,32,256]{2,1,0:T(8,128)(2,1)S(1)} %get-tuple-element.200), channel_id=1, source_target_pairs={{1,3},{3,5},{5,7},{7,9},{9,11},{11,13},{13,15},{15,17},{17,19},{19... | collective-permute-start | bytes 49160 | tf_op jit(solution)/shard_map/ppermute | solution.py:410
  119.1 5.3 %collective-permute-start.49 = (bf16[9,32,128]{2,1,0:T(8,128)(2,1)S(1)}, bf16[9,32,128]{2,1,0:T(8,128)(2,1)S(1)}, u32[]{:S(2)}, u32[]{:S(2)}) collective-permute-start(bf16[9,32,128]{2,1,0:T(8,128)(2,1)S(1)} %get-tuple-element.206), channel_id=1, source_target_pairs={{0,16},{1,17},{2,18},{3,19},{4,20},{5,21},{6,22},{7,23},{8,24},{9,... | collective-permute-start | bytes 221192 | tf_op jit(solution)/shard_map/ppermute | solution.py:260
  120.9 1.2 collective-permute-start.50
  120.9 1.3 %collective-permute-start.51 = (bf16[1,32,256]{2,1,0:T(8,128)(2,1)S(1)}, bf16[1,32,256]{2,1,0:T(8,128)(2,1)S(1)}, u32[]{:S(2)}, u32[]{:S(2)}) collective-permute-start(bf16[1,32,256]{2,1,0:T(8,128)(2,1)S(1)} %collective-permute-done.48), channel_id=1, source_target_pairs={{0,1},{1,0},{2,3},{3,2},{4,5},{5,4},{6,7},{7,6},{8,9},{9,8},{10,11... | collective-permute-start | bytes 49160 | tf_op jit(solution)/shard_map/ppermute | solution.py:269
  (1 other events, 0.8 us)

commit v18 on v17

--- a/solution.py
+++ b/solution.py
@@ -95,14 +95,9 @@
 
 def couple_kernel(source_ref, target_ref, coupling_ref, *refs, order, unroll):
     chips = sum(len(group) for group in order)
+    in_refs, out_refs, (sources, total) = refs[: 2 * chips], refs[2 * chips : -2], refs[-2:]
     blocks, rank_top, _ = coupling_ref.shape
-    near_size, far, mains, rhs, _ = refs[0].shape
-    per_core = 1 + chips - near_size
-    in_refs, out_refs, (sources, total) = [], refs[2 * per_core : -2], refs[-2:]
-    for core in range(2):
-        joined, *single = refs[core * per_core : (core + 1) * per_core]
-        pieces = {chip: joined.at[place] for place, chip in enumerate(order[1])} | dict(zip(order[0], single))
-        in_refs += [pieces[chip] for chip in range(chips)]
+    far, mains, rhs, _ = in_refs[0].shape
     quads = mains // 3
     clusters = mains + quads
 
@@ -306,7 +301,7 @@
     couple = pl.pallas_call(
         functools.partial(couple_kernel, order=order, unroll=64),
         out_shape=[shape((4, far) + tile_shape, BF)] * 4,
-        in_specs=[SMEM, SMEM, VMEM] + [VMEM] * (cores * (1 + len(order[0]))),
+        in_specs=[SMEM, SMEM, VMEM] + [VMEM] * (cores * chips),
         out_specs=[VMEM] * 4,
         scratch_shapes=[
             pltpu.VMEM((devices * clusters, rhs, LANES), BF),
@@ -354,7 +349,6 @@
 
     own_shape = shape((far,) + tile_shape, F32)
     join = adder(join_kernel, far, [part_shape])
-    join_near = adder(join_kernel, 4, [shape((4,) + part_shape.shape, BF)])
     relaid = pl.pallas_call(
         order_kernel,
         out_shape=shape((8, LANES), F32),
@@ -392,13 +386,19 @@
         got = {0: column, x: swap(column, x), y: swap(column, y), z: swap(column, z)}
         near_sum = near(field_in, near_field)
         got, near_sum = barrier((got, near_sum))
-        corner = swap(got[x], y | z)
-        (near_pieces,) = join_near(*[got[chip] for chip in order[1]])
+        corner = swap(column, x | y | z)
+        other = {chip: swap_cores(part) for chip, part in got.items()}
         got |= {x | y: swap(got[x], y), y | z: swap(got[y], z), z | x: swap(got[z], x)}
+        got, corner, outer = barrier((got, corner, lax.ppermute(outer, "clu", halo_pairs)))
         got[x | y | z] = corner
-        far_pieces, other_near = barrier(([got[chip] for chip in order[0]], swap_cores(near_pieces)))
-        other_far = [swap_cores(part) for part in far_pieces]
-        totals = couple(source_rows, target_rows, coupling, near_pieces, *far_pieces, other_near, *other_far)
+        other |= {chip: swap_cores(got[chip]) for chip in order[0]}
+        totals = couple(
+            source_rows,
+            target_rows,
+            coupling,
+            *[got[chip] for chip in range(chips)],
+            *[other[chip] for chip in range(chips)],
+        )
         keep_long, keep, send_long, send = totals
         corner, xy, yz, zx = far_add(keep_long, swap_cores(send_long))
         corner, xy, yz, zx, send = barrier((corner, xy, yz, zx, send))
@@ -406,11 +406,11 @@
         own, to_x, to_y, to_z, inner, outer = barrier(
             (*middle_add(keep, swapped, to_x, to_y, to_z), inner, outer)
         )
+        edges = edge(swap_cores(inner), swap_cores(outer), near_field, near_field)
         parts = [swap(to_x, x), swap(to_y, y), swap(to_z, z), swap(corner, x | y | z)]
-        own, parts, inner, outer = barrier((own, parts, inner, lax.ppermute(outer, "clu", halo_pairs)))
+        own, parts, edges = barrier((own, parts, edges))
         total, *away = last_add(own, *parts)
-        edges = edge(swap_cores(inner), swap_cores(outer), near_field, near_field)
-        terms, edges = barrier(([swap_far(part, s + 1) for s, part in enumerate(away)], edges))
+        terms = [swap_far(part, s + 1) for s, part in enumerate(away)]
         return finish(with_coeffs)(ranks, near_sum, edges, basis, transfer, total, *terms)
 
     first, *second_args = apply_matrix(charges, first_coeffs, inner, outer, coupling, True)

time: 126 us -> 128 us (1.016)
  starting transfers between devices: 50.3 us -> 57.4 us
  waiting for transfers between devices: 52 us -> 47 us
    ppermute x2, waiting for transfers between devices: 8.64 us -> 0.01 us  [apply_matrix(): lax.ppermute(outer, 'clu', halo_pairs)]
    ppermute x28, starting transfers between devices: 35.7 us -> 39.2 us  [swap(): lax.ppermute(part, 'clu', [(d, d ^ (turned if d % cores else direction) *...]
    ppermute x4, starting transfers between devices: 7.51 us -> 10.6 us  [swap_far(): lax.ppermute(part, 'clu', [(d, (d + shift * cube) % devices) for d in ran...]
    ppermute x18 -> x24, waiting for transfers between devices: 7.58 us -> 9.92 us  [swap_cores(): return lax.ppermute(part, 'clu', [(d, d ^ 1) for d in range(devices)])]
    ppermute x18 -> x24, starting transfers between devices: 4.49 us -> 5.01 us  [swap_cores(): return lax.ppermute(part, 'clu', [(d, d ^ 1) for d in range(devices)])]
    pallas_call x4 -> x2, Pallas kernels: 7.29 us -> 7.21 us  [apply_matrix(): couple(source_rows, target_rows, coupling, *[got[chip] for chip in range(...]
  transfers between devices with their start and end apart: 52 -> 58, of which waited for: 38 -> 33; matrix products, arithmetic and copies ran while one was open for 4% -> 4% of each run, Pallas kernels for 2% -> 2%
where the time goes in v18:
time: 128 us
  starting transfers between devices  57.4 us (45%)
  waiting for transfers between devices  47 us (37%)
  Pallas kernels  16.2 us (13%)
  local copies, waits for them, and re-layouts  6.54 us (5%)
    ppermute x28, starting transfers between devices, swap(): lax.ppermute(part, 'clu', [(d, d ^ (turned if d % cores else direction) *...  39.2 us
    ppermute x28, waiting for transfers between devices, swap(): lax.ppermute(part, 'clu', [(d, d ^ (turned if d % cores else direction) *...  25.7 us
    ppermute x4, waiting for transfers between devices, swap_far(): lax.ppermute(part, 'clu', [(d, (d + shift * cube) % devices) for d in ran...  11.4 us
    ppermute x4, starting transfers between devices, swap_far(): lax.ppermute(part, 'clu', [(d, (d + shift * cube) % devices) for d in ran...  10.6 us
    ppermute x24, waiting for transfers between devices, swap_cores(): return lax.ppermute(part, 'clu', [(d, d ^ 1) for d in range(devices)])  9.92 us
    pallas_call x2, Pallas kernels, apply_matrix(): couple(source_rows, target_rows, coupling, *[got[chip] for chip in range(...  7.21 us
    unnamed x27, local copies, waits for them, and re-layouts  6.54 us
    ppermute x24, starting transfers between devices, swap_cores(): return lax.ppermute(part, 'clu', [(d, d ^ 1) for d in range(devices)])  5.01 us
  transfers between devices with their start and end apart: 58, of which 33 were waited for; matrix products, arithmetic and copies ran while one was open for 4% of the time, Pallas kernels for 2%

profile of v18, /device:TPU:0, one launch (start us, length us, event | category | flops | bytes accessed | tf_op | source)
XLA Modules:
  0.0 128.0 jit_solution(9530557702992829124)
XLA Ops:
  0.6 2.9 %shard_map.95 = (bf16[9,32,128]{2,1,0:T(8,128)(2,1)}, bf16[1,32,256]{2,1,0:T(8,128)(2,1)}, bf16[1,32,256]{2,1,0:T(8,128)(2,1)}) custom-call(s32[12]{0:T(128)} %ranks_ref.5, bf16[8,32,256]{2,1,0:T(8,128)(2,1)} %v_ref.1, bf16[8,96,256]{2,1,0:T(8,128)(2,1)} %basis_ref.3, bf16[8,96,96]{2,1,0:T(8,128)(2,1)} %transfer_ref.3), custom_call_target="tpu_custom_call" | custom-call | tf_op jit(solution)/shard_map/pallas_call | solution.py:287
  3.6 4.1 %collective-permute-start = (bf16[9,32,128]{2,1,0:T(8,128)(2,1)}, bf16[9,32,128]{2,1,0:T(8,128)(2,1)S(1)}, u32[]{:S(2)}, u32[]{:S(2)}) collective-permute-start(bf16[9,32,128]{2,1,0:T(8,128)(2,1)} %get-tuple-element.109.__.refs_0_), channel_id=1, source_target_pairs={{0,16},{1,17},{2,18},{3,19},{4,20},{5,21},{6,22},{7,23},{8,24},{9,... | collective-permute-start | bytes 221192 | tf_op jit(solution)/shard_map/ppermute | solution.py:255
  7.7 4.8 %copy.10._.coupling_ref = bf16[128,96,96]{2,1,0:T(8,128)(2,1)} copy(bf16[128,96,96]{0,2,1:T(8,128)(2,1)} %param.12) | data formatting | bytes 4718592 | tf_op args[4]
  12.4 0.6 shard_map.96._
  13.0 0.8 copy-done.7
  13.9 1.6 %collective-permute-start.3 = (bf16[2,9,32,128]{3,2,1,0:T(8,128)(2,1)S(1)}, bf16[2,9,32,128]{3,2,1,0:T(8,128)(2,1)S(1)}, u32[]{:S(2)}, u32[]{:S(2)}) collective-permute-start(bf16[2,9,32,128]{3,2,1,0:T(8,128)(2,1)S(1)} %shard_map.97.refs_0_), channel_id=1, source_target_pairs={{0,8},{1,3},{2,10},{3,1},{4,12},{5,7},{6,14},{7,5},{8,0},{9,11},{1... | collective-permute-start | bytes 442376 | tf_op jit(solution)/shard_map/ppermute | solution.py:259
  15.5 1.5 %collective-permute-start.2 = (bf16[2,9,32,128]{3,2,1,0:T(8,128)(2,1)S(1)}, bf16[2,9,32,128]{3,2,1,0:T(8,128)(2,1)S(1)}, u32[]{:S(2)}, u32[]{:S(2)}) collective-permute-start(bf16[2,9,32,128]{3,2,1,0:T(8,128)(2,1)S(1)} %shard_map.97.refs_0_), channel_id=1, source_target_pairs={{0,4},{1,9},{2,6},{3,11},{4,0},{5,13},{6,2},{7,15},{8,12},{9,1},{1... | collective-permute-start | bytes 442376 | tf_op jit(solution)/shard_map/ppermute | solution.py:259
  17.0 1.5 %collective-permute-start.1 = (bf16[2,9,32,128]{3,2,1,0:T(8,128)(2,1)S(1)}, bf16[2,9,32,128]{3,2,1,0:T(8,128)(2,1)S(1)}, u32[]{:S(2)}, u32[]{:S(2)}) collective-permute-start(bf16[2,9,32,128]{3,2,1,0:T(8,128)(2,1)S(1)} %shard_map.97.refs_0_), channel_id=1, source_target_pairs={{0,2},{1,5},{2,0},{3,7},{4,6},{5,1},{6,4},{7,3},{8,10},{9,13},{10,... | collective-permute-start | bytes 442376 | tf_op jit(solution)/shard_map/ppermute | solution.py:259
  18.5 0.6 shard_map.98.near_ref
  19.5 1.0 collective-permute-done.3.refs_4_
  20.5 1.9 %collective-permute-done.2.refs_2_ = bf16[2,9,32,128]{3,2,1,0:T(8,128)(2,1)S(1)} collective-permute-done((bf16[2,9,32,128]{3,2,1,0:T(8,128)(2,1)S(1)}, bf16[2,9,32,128]{3,2,1,0:T(8,128)(2,1)S(1)}, u32[]{:S(2)}, u32[]{:S(2)}) %collective-permute-start.2) | collective-permute-done | bytes 147488 | tf_op jit(solution)/shard_map/ppermute | solution.py:259
  22.4 1.9 %collective-permute-done.1.refs_1_ = bf16[2,9,32,128]{3,2,1,0:T(8,128)(2,1)S(1)} collective-permute-done((bf16[2,9,32,128]{3,2,1,0:T(8,128)(2,1)S(1)}, bf16[2,9,32,128]{3,2,1,0:T(8,128)(2,1)S(1)}, u32[]{:S(2)}, u32[]{:S(2)}) %collective-permute-start.1) | collective-permute-done | bytes 147488 | tf_op jit(solution)/shard_map/ppermute | solution.py:259
  24.9 1.3 %collective-permute-start.8 = (bf16[1,32,256]{2,1,0:T(8,128)(2,1)S(1)}, bf16[1,32,256]{2,1,0:T(8,128)(2,1)S(1)}, u32[]{:S(2)}, u32[]{:S(2)}) collective-permute-start(bf16[1,32,256]{2,1,0:T(8,128)(2,1)S(1)} %copy-done.12), channel_id=1, source_target_pairs={{1,3},{3,5},{5,7},{7,9},{9,11},{11,13},{13,15},{15,17},{17,19},{19... | collective-permute-start | bytes 49160 | tf_op jit(solution)/shard_map/ppermute | solution.py:392
  26.1 5.6 %collective-permute-start.6 = (bf16[2,9,32,128]{3,2,1,0:T(8,128)(2,1)S(1)}, bf16[2,9,32,128]{3,2,1,0:T(8,128)(2,1)S(1)}, u32[]{:S(2)}, u32[]{:S(2)}) collective-permute-start(bf16[2,9,32,128]{3,2,1,0:T(8,128)(2,1)S(1)} %collective-permute-done.2.refs_2_), channel_id=1, source_target_pairs={{0,8},{1,3},{2,10},{3,1},{4,12},{5,7},{6,14},{7,5},{8,0},{9,11},{1... | collective-permute-start | bytes 442376 | tf_op jit(solution)/shard_map/ppermute | solution.py:259
  32.3 2.6 %collective-permute-done.6.refs_6_ = bf16[2,9,32,128]{3,2,1,0:T(8,128)(2,1)S(1)} collective-permute-done((bf16[2,9,32,128]{3,2,1,0:T(8,128)(2,1)S(1)}, bf16[2,9,32,128]{3,2,1,0:T(8,128)(2,1)S(1)}, u32[]{:S(2)}, u32[]{:S(2)}) %collective-permute-start.6) | collective-permute-done | bytes 147488 | tf_op jit(solution)/shard_map/ppermute | solution.py:259
  34.9 1.9 %collective-permute-done.5.refs_5_ = bf16[2,9,32,128]{3,2,1,0:T(8,128)(2,1)S(1)} collective-permute-done((bf16[2,9,32,128]{3,2,1,0:T(8,128)(2,1)S(1)}, bf16[2,9,32,128]{3,2,1,0:T(8,128)(2,1)S(1)}, u32[]{:S(2)}, u32[]{:S(2)}) %collective-permute-start.5) | collective-permute-done | bytes 147488 | tf_op jit(solution)/shard_map/ppermute | solution.py:259
  36.9 0.5 collective-permute-start.14
  39.0 3.6 %shard_map.100 = (bf16[4,2,9,32,128]{4,3,2,1,0:T(8,128)(2,1)S(1)}, bf16[4,2,9,32,128]{4,3,2,1,0:T(8,128)(2,1)S(1)}, bf16[4,2,9,32,128]{4,3,2,1,0:T(8,128)(2,1)S(1)}, bf16[4,2,9,32,128]{4,3,2,1,0:T(8,128)(2,1)S(1)}) custom-call(s32[128]{0:T(128)S(1)} %bitcast.4, s32[128]{0:T(128)S(1)} %bitcast.6, bf16[128,96,96]{2,1,0:T(8,128)(2,1)S(1)} %copy-done.1, ...), custom_call_target="tpu_custom_call" | custom-call | flops 75497472 | bytes 10485760 | tf_op jit(solution)/shard_map/pallas_call | solution.py:395
  43.0 1.7 %collective-permute-done.17.swap_ref = bf16[4,2,9,32,128]{4,3,2,1,0:T(8,128)(2,1)S(1)} collective-permute-done((bf16[4,2,9,32,128]{4,3,2,1,0:T(8,128)(2,1)S(1)}, bf16[4,2,9,32,128]{4,3,2,1,0:T(8,128)(2,1)S(1)}, u32[]{:S(2)}, u32[]{:S(2)}) %collective-permute-start.17) | collective-permute-done | bytes 589856 | tf_op jit(solution)/shard_map/ppermute | solution.py:264
  45.2 1.1 collective-permute-start.19
  46.3 3.8 %collective-permute-start.25 = (bf16[2,9,32,128]{3,2,1,0:T(8,128)(2,1)S(1)}, bf16[2,9,32,128]{3,2,1,0:T(8,128)(2,1)S(1)}, u32[]{:S(2)}, u32[]{:S(2)}) collective-permute-start(bf16[2,9,32,128]{3,2,1,0:T(8,128)(2,1)S(1)} %get-tuple-element.152), channel_id=1, source_target_pairs={{0,14},{1,15},{2,12},{3,13},{4,10},{5,11},{6,8},{7,9},{8,6},{9,7},... | collective-permute-start | bytes 442376 | tf_op jit(solution)/shard_map/ppermute | solution.py:259
  50.1 1.9 %collective-permute-done.18.refs_0_ = bf16[2,9,32,128]{3,2,1,0:T(8,128)(2,1)S(1)} collective-permute-done((bf16[2,9,32,128]{3,2,1,0:T(8,128)(2,1)S(1)}, bf16[2,9,32,128]{3,2,1,0:T(8,128)(2,1)S(1)}, u32[]{:S(2)}, u32[]{:S(2)}) %collective-permute-start.18) | collective-permute-done | bytes 147488 | tf_op jit(solution)/shard_map/ppermute | solution.py:259
  52.0 2.5 %collective-permute-done.20.refs_2_ = bf16[2,9,32,128]{3,2,1,0:T(8,128)(2,1)S(1)} collective-permute-done((bf16[2,9,32,128]{3,2,1,0:T(8,128)(2,1)S(1)}, bf16[2,9,32,128]{3,2,1,0:T(8,128)(2,1)S(1)}, u32[]{:S(2)}, u32[]{:S(2)}) %collective-permute-start.20) | collective-permute-done | bytes 147488 | tf_op jit(solution)/shard_map/ppermute | solution.py:259
  54.8 1.2 collective-permute-start.23
  56.0 1.8 %collective-permute-start.24 = (bf16[2,9,32,128]{3,2,1,0:T(8,128)(2,1)S(1)}, bf16[2,9,32,128]{3,2,1,0:T(8,128)(2,1)S(1)}, u32[]{:S(2)}, u32[]{:S(2)}) collective-permute-start(bf16[2,9,32,128]{3,2,1,0:T(8,128)(2,1)S(1)} %get-tuple-element.151), channel_id=1, source_target_pairs={{0,8},{1,3},{2,10},{3,1},{4,12},{5,7},{6,14},{7,5},{8,0},{9,11},{1... | collective-permute-start | bytes 442376 | tf_op jit(solution)/shard_map/ppermute | solution.py:259
  57.8 1.2 collective-permute-done.26.inner_ref
  59.2 1.0 collective-permute-done.27.outer_ref
  60.4 0.9 collective-permute-done.22.refs_0_
  61.3 1.7 %collective-permute-start.28 = (bf16[9,32,128]{2,1,0:T(8,128)(2,1)S(1)}, bf16[9,32,128]{2,1,0:T(8,128)(2,1)S(1)}, u32[]{:S(2)}, u32[]{:S(2)}) collective-permute-start(bf16[9,32,128]{2,1,0:T(8,128)(2,1)S(1)} %get-tuple-element.162), channel_id=1, source_target_pairs={{0,16},{1,17},{2,18},{3,19},{4,20},{5,21},{6,22},{7,23},{8,24},{9,... | collective-permute-start | bytes 221192 | tf_op jit(solution)/shard_map/ppermute | solution.py:255
  63.0 3.6 %collective-permute-done.28.rest_0_ = bf16[9,32,128]{2,1,0:T(8,128)(2,1)S(1)} collective-permute-done((bf16[9,32,128]{2,1,0:T(8,128)(2,1)S(1)}, bf16[9,32,128]{2,1,0:T(8,128)(2,1)S(1)}, u32[]{:S(2)}, u32[]{:S(2)}) %collective-permute-start.28) | collective-permute-done | bytes 73760 | tf_op jit(solution)/shard_map/ppermute | solution.py:255
  66.7 1.6 %shard_map.105 = (bf16[8,32,256]{2,1,0:T(8,128)(2,1)}, bf16[9,32,128]{2,1,0:T(8,128)(2,1)S(1)}, bf16[1,32,256]{2,1,0:T(8,128)(2,1)S(1)}, bf16[1,32,256]{2,1,0:T(8,128)(2,1)S(1)}) custom-call(s32[12]{0:T(128)S(1)} %copy-done.8, f32[8,32,256]{2,1,0:T(8,128)S(1)} %shard_map.98.near_ref, f32[2,32,256]{2,1,0:T(8,128)S(1)} %shard_map.103.edge_ref, ...), custom_call_target="tpu_custom_call" | custom-call | tf_op jit(solution)/shard_map/pallas_call | solution.py:414
  68.3 1.6 %collective-permute-start.29 = (bf16[9,32,128]{2,1,0:T(8,128)(2,1)S(1)}, bf16[9,32,128]{2,1,0:T(8,128)(2,1)S(1)}, u32[]{:S(2)}, u32[]{:S(2)}) collective-permute-start(bf16[9,32,128]{2,1,0:T(8,128)(2,1)S(1)} %get-tuple-element.164.refs_0_), channel_id=1, source_target_pairs={{0,16},{1,17},{2,18},{3,19},{4,20},{5,21},{6,22},{7,23},{8,24},{9,... | collective-permute-start | bytes 221192 | tf_op jit(solution)/shard_map/ppermute | solution.py:255
  69.9 3.6 %collective-permute-done.29.refs_1_ = bf16[9,32,128]{2,1,0:T(8,128)(2,1)S(1)} collective-permute-done((bf16[9,32,128]{2,1,0:T(8,128)(2,1)S(1)}, bf16[9,32,128]{2,1,0:T(8,128)(2,1)S(1)}, u32[]{:S(2)}, u32[]{:S(2)}) %collective-permute-start.29) | collective-permute-done | bytes 73760 | tf_op jit(solution)/shard_map/ppermute | solution.py:255
  73.5 1.8 %collective-permute-start.32 = (bf16[2,9,32,128]{3,2,1,0:T(8,128)(2,1)S(1)}, bf16[2,9,32,128]{3,2,1,0:T(8,128)(2,1)S(1)}, u32[]{:S(2)}, u32[]{:S(2)}) collective-permute-start(bf16[2,9,32,128]{3,2,1,0:T(8,128)(2,1)S(1)} %shard_map.106.refs_0_), channel_id=1, source_target_pairs={{0,8},{1,3},{2,10},{3,1},{4,12},{5,7},{6,14},{7,5},{8,0},{9,11},{1... | collective-permute-start | bytes 442376 | tf_op jit(solution)/shard_map/ppermute | solution.py:259
  75.3 1.0 collective-permute-start.31
  76.3 1.5 %collective-permute-start.30 = (bf16[2,9,32,128]{3,2,1,0:T(8,128)(2,1)S(1)}, bf16[2,9,32,128]{3,2,1,0:T(8,128)(2,1)S(1)}, u32[]{:S(2)}, u32[]{:S(2)}) collective-permute-start(bf16[2,9,32,128]{3,2,1,0:T(8,128)(2,1)S(1)} %shard_map.106.refs_0_), channel_id=1, source_target_pairs={{0,2},{1,5},{2,0},{3,7},{4,6},{5,1},{6,4},{7,3},{8,10},{9,13},{10,... | collective-permute-start | bytes 442376 | tf_op jit(solution)/shard_map/ppermute | solution.py:259
  77.9 0.9 copy-done.6
  78.8 0.6 shard_map.107.near_ref
  79.4 2.1 %collective-permute-start.36 = (bf16[2,9,32,128]{3,2,1,0:T(8,128)(2,1)S(1)}, bf16[2,9,32,128]{3,2,1,0:T(8,128)(2,1)S(1)}, u32[]{:S(2)}, u32[]{:S(2)}) collective-permute-start(bf16[2,9,32,128]{3,2,1,0:T(8,128)(2,1)S(1)} %shard_map.106.refs_0_), channel_id=1, source_target_pairs={{0,14},{1,15},{2,12},{3,13},{4,10},{5,11},{6,8},{7,9},{8,6},{9,7},... | collective-permute-start | bytes 442376 | tf_op jit(solution)/shard_map/ppermute | solution.py:259
  81.6 0.6 collective-permute-done.30.refs_1_
  82.2 1.4 %collective-permute-start.33 = (bf16[2,9,32,128]{3,2,1,0:T(8,128)(2,1)S(1)}, bf16[2,9,32,128]{3,2,1,0:T(8,128)(2,1)S(1)}, u32[]{:S(2)}, u32[]{:S(2)}) collective-permute-start(bf16[2,9,32,128]{3,2,1,0:T(8,128)(2,1)S(1)} %collective-permute-done.30.refs_1_), channel_id=1, source_target_pairs={{0,4},{1,9},{2,6},{3,11},{4,0},{5,13},{6,2},{7,15},{8,12},{9,1},{1... | collective-permute-start | bytes 442376 | tf_op jit(solution)/shard_map/ppermute | solution.py:259
  83.5 1.3 %collective-permute-start.37 = (bf16[1,32,256]{2,1,0:T(8,128)(2,1)S(1)}, bf16[1,32,256]{2,1,0:T(8,128)(2,1)S(1)}, u32[]{:S(2)}, u32[]{:S(2)}) collective-permute-start(bf16[1,32,256]{2,1,0:T(8,128)(2,1)S(1)} %get-tuple-element.170), channel_id=1, source_target_pairs={{1,3},{3,5},{5,7},{7,9},{9,11},{11,13},{13,15},{15,17},{17,19},{19... | collective-permute-start | bytes 49160 | tf_op jit(solution)/shard_map/ppermute | solution.py:392
  84.8 3.9 %collective-permute-start.35 = (bf16[2,9,32,128]{3,2,1,0:T(8,128)(2,1)S(1)}, bf16[2,9,32,128]{3,2,1,0:T(8,128)(2,1)S(1)}, u32[]{:S(2)}, u32[]{:S(2)}) collective-permute-start(bf16[2,9,32,128]{3,2,1,0:T(8,128)(2,1)S(1)} %collective-permute-done.31.refs_2_), channel_id=1, source_target_pairs={{0,8},{1,3},{2,10},{3,1},{4,12},{5,7},{6,14},{7,5},{8,0},{9,11},{1... | collective-permute-start | bytes 442376 | tf_op jit(solution)/shard_map/ppermute | solution.py:259
  88.7 0.6 collective-permute-start.34
  89.9 2.0 %collective-permute-done.35.refs_6_ = bf16[2,9,32,128]{3,2,1,0:T(8,128)(2,1)S(1)} collective-permute-done((bf16[2,9,32,128]{3,2,1,0:T(8,128)(2,1)S(1)}, bf16[2,9,32,128]{3,2,1,0:T(8,128)(2,1)S(1)}, u32[]{:S(2)}, u32[]{:S(2)}) %collective-permute-start.35) | collective-permute-done | bytes 147488 | tf_op jit(solution)/shard_map/ppermute | solution.py:259
  91.9 1.9 %collective-permute-done.34.refs_5_ = bf16[2,9,32,128]{3,2,1,0:T(8,128)(2,1)S(1)} collective-permute-done((bf16[2,9,32,128]{3,2,1,0:T(8,128)(2,1)S(1)}, bf16[2,9,32,128]{3,2,1,0:T(8,128)(2,1)S(1)}, u32[]{:S(2)}, u32[]{:S(2)}) %collective-permute-start.34) | collective-permute-done | bytes 147488 | tf_op jit(solution)/shard_map/ppermute | solution.py:259
  93.9 0.5 collective-permute-start.43
  96.0 3.6 %shard_map.108 = (bf16[4,2,9,32,128]{4,3,2,1,0:T(8,128)(2,1)S(1)}, bf16[4,2,9,32,128]{4,3,2,1,0:T(8,128)(2,1)S(1)}, bf16[4,2,9,32,128]{4,3,2,1,0:T(8,128)(2,1)S(1)}, bf16[4,2,9,32,128]{4,3,2,1,0:T(8,128)(2,1)S(1)}) custom-call(s32[128]{0:T(128)S(1)} %bitcast.5, s32[128]{0:T(128)S(1)} %bitcast.7, bf16[128,96,96]{2,1,0:T(8,128)(2,1)S(1)} %copy-done.1, ...), custom_call_target="tpu_custom_call" | custom-call | flops 75497472 | bytes 10485760 | tf_op jit(solution)/shard_map/pallas_call | solution.py:395
  99.9 1.7 %collective-permute-done.46.swap_ref = bf16[4,2,9,32,128]{4,3,2,1,0:T(8,128)(2,1)S(1)} collective-permute-done((bf16[4,2,9,32,128]{4,3,2,1,0:T(8,128)(2,1)S(1)}, bf16[4,2,9,32,128]{4,3,2,1,0:T(8,128)(2,1)S(1)}, u32[]{:S(2)}, u32[]{:S(2)}) %collective-permute-start.46) | collective-permute-done | bytes 589856 | tf_op jit(solution)/shard_map/ppermute | solution.py:264
  102.1 1.3 collective-permute-start.47
  103.4 0.7 collective-permute-start.48
  104.2 0.6 collective-permute-start.49
  104.7 2.4 %collective-permute-start.54 = (bf16[2,9,32,128]{3,2,1,0:T(8,128)(2,1)S(1)}, bf16[2,9,32,128]{3,2,1,0:T(8,128)(2,1)S(1)}, u32[]{:S(2)}, u32[]{:S(2)}) collective-permute-start(bf16[2,9,32,128]{3,2,1,0:T(8,128)(2,1)S(1)} %get-tuple-element.205), channel_id=1, source_target_pairs={{0,14},{1,15},{2,12},{3,13},{4,10},{5,11},{6,8},{7,9},{8,6},{9,7},... | collective-permute-start | bytes 442376 | tf_op jit(solution)/shard_map/ppermute | solution.py:259
  107.1 1.5 %collective-permute-done.47.refs_0_ = bf16[2,9,32,128]{3,2,1,0:T(8,128)(2,1)S(1)} collective-permute-done((bf16[2,9,32,128]{3,2,1,0:T(8,128)(2,1)S(1)}, bf16[2,9,32,128]{3,2,1,0:T(8,128)(2,1)S(1)}, u32[]{:S(2)}, u32[]{:S(2)}) %collective-permute-start.47) | collective-permute-done | bytes 147488 | tf_op jit(solution)/shard_map/ppermute | solution.py:259
  108.6 1.3 %collective-permute-done.48.refs_1_ = bf16[2,9,32,128]{3,2,1,0:T(8,128)(2,1)S(1)} collective-permute-done((bf16[2,9,32,128]{3,2,1,0:T(8,128)(2,1)S(1)}, bf16[2,9,32,128]{3,2,1,0:T(8,128)(2,1)S(1)}, u32[]{:S(2)}, u32[]{:S(2)}) %collective-permute-start.48) | collective-permute-done | bytes 147488 | tf_op jit(solution)/shard_map/ppermute | solution.py:259
  109.9 2.4 %collective-permute-done.49.refs_2_ = bf16[2,9,32,128]{3,2,1,0:T(8,128)(2,1)S(1)} collective-permute-done((bf16[2,9,32,128]{3,2,1,0:T(8,128)(2,1)S(1)}, bf16[2,9,32,128]{3,2,1,0:T(8,128)(2,1)S(1)}, u32[]{:S(2)}, u32[]{:S(2)}) %collective-permute-start.49) | collective-permute-done | bytes 147488 | tf_op jit(solution)/shard_map/ppermute | solution.py:259
  112.6 0.8 collective-permute-start.52
  113.4 2.0 %collective-permute-start.53 = (bf16[2,9,32,128]{3,2,1,0:T(8,128)(2,1)S(1)}, bf16[2,9,32,128]{3,2,1,0:T(8,128)(2,1)S(1)}, u32[]{:S(2)}, u32[]{:S(2)}) collective-permute-start(bf16[2,9,32,128]{3,2,1,0:T(8,128)(2,1)S(1)} %get-tuple-element.204), channel_id=1, source_target_pairs={{0,8},{1,3},{2,10},{3,1},{4,12},{5,7},{6,14},{7,5},{8,0},{9,11},{1... | collective-permute-start | bytes 442376 | tf_op jit(solution)/shard_map/ppermute | solution.py:259
  115.4 1.2 collective-permute-done.55.inner_ref
  116.7 1.0 collective-permute-done.56.outer_ref
  117.9 1.1 collective-permute-done.51.refs_0_
  119.1 3.2 %collective-permute-start.57 = (bf16[9,32,128]{2,1,0:T(8,128)(2,1)S(1)}, bf16[9,32,128]{2,1,0:T(8,128)(2,1)S(1)}, u32[]{:S(2)}, u32[]{:S(2)}) collective-permute-start(bf16[9,32,128]{2,1,0:T(8,128)(2,1)S(1)} %get-tuple-element.215), channel_id=1, source_target_pairs={{0,16},{1,17},{2,18},{3,19},{4,20},{5,21},{6,22},{7,23},{8,24},{9,... | collective-permute-start | bytes 221192 | tf_op jit(solution)/shard_map/ppermute | solution.py:255
  122.3 4.1 %collective-permute-done.57.rest_0_ = bf16[9,32,128]{2,1,0:T(8,128)(2,1)S(1)} collective-permute-done((bf16[9,32,128]{2,1,0:T(8,128)(2,1)S(1)}, bf16[9,32,128]{2,1,0:T(8,128)(2,1)S(1)}, u32[]{:S(2)}, u32[]{:S(2)}) %collective-permute-start.57) | collective-permute-done | bytes 73760 | tf_op jit(solution)/shard_map/ppermute | solution.py:255
  126.4 1.6 %shard_map.113 = bf16[8,32,256]{2,1,0:T(8,128)(2,1)} custom-call(s32[12]{0:T(128)S(1)} %copy-done.8, f32[8,32,256]{2,1,0:T(8,128)S(1)} %shard_map.107.near_ref, f32[2,32,256]{2,1,0:T(8,128)S(1)} %shard_map.111.edge_ref, bf16[8,96,256]{2,1,0:T(8,128)(2,1)S(1)} %copy-done.2, bf16[8,96,96]{2,1,0:T(8,128)(2,1)S(1)} %copy-done.3, ...), custom_call_target="tpu_custom_call" | custom-call | tf_op jit(solution)/shard_map/pallas_call | solution.py:414
  (98 shorter events, 8.6 us)
Async XLA Ops:
  3.5 15.0 %copy-start = (bf16[8,3,256,256]{3,2,1,0:T(8,128)(2,1)S(1)}, bf16[8,3,256,256]{3,2,1,0:T(8,128)(2,1)}, u32[]{:S(2)}) copy-start(bf16[8,3,256,256]{3,2,1,0:T(8,128)(2,1)} %last_ref.3) | copy-start | bytes 9437188
  3.6 15.0 %copy-start.4 = (bf16[8,32,256]{2,1,0:T(8,128)(2,1)S(1)}, bf16[8,32,256]{2,1,0:T(8,128)(2,1)}, u32[]{:S(2)}) copy-start(bf16[8,32,256]{2,1,0:T(8,128)(2,1)} %v_ref.1) | copy-start | bytes 393220
  3.6 9.5 %collective-permute-start = (bf16[9,32,128]{2,1,0:T(8,128)(2,1)}, bf16[9,32,128]{2,1,0:T(8,128)(2,1)S(1)}, u32[]{:S(2)}, u32[]{:S(2)}) collective-permute-start(bf16[9,32,128]{2,1,0:T(8,128)(2,1)} %get-tuple-element.109.__.refs_0_), channel_id=1, source_target_pairs={{0,16},{1,17},{2,18},{3,19},{4,20},{5,21},{6,22},{7,23},{8,24},{9,... | collective-permute-start | bytes 221192 | tf_op jit(solution)/shard_map/ppermute | solution.py:255
  12.4 25.5 %copy-start.9 = (s32[128]{0:T(128)S(1)}, s32[128]{0:T(128)}, u32[]{:S(2)}) copy-start(s32[128]{0:T(128)} %param.14) | copy-start | bytes 1540
  12.4 25.5 %copy-start.10 = (s32[128]{0:T(128)S(1)}, s32[128]{0:T(128)}, u32[]{:S(2)}) copy-start(s32[128]{0:T(128)} %param.15) | copy-start | bytes 1540
  13.0 26.0 %copy-start.1 = (bf16[128,96,96]{2,1,0:T(8,128)(2,1)S(1)}, bf16[128,96,96]{2,1,0:T(8,128)(2,1)}, u32[]{:S(2)}) copy-start(bf16[128,96,96]{2,1,0:T(8,128)(2,1)} %copy.10._.coupling_ref) | copy-start | bytes 7077892
  13.9 6.6 %collective-permute-start.3 = (bf16[2,9,32,128]{3,2,1,0:T(8,128)(2,1)S(1)}, bf16[2,9,32,128]{3,2,1,0:T(8,128)(2,1)S(1)}, u32[]{:S(2)}, u32[]{:S(2)}) collective-permute-start(bf16[2,9,32,128]{3,2,1,0:T(8,128)(2,1)S(1)} %shard_map.97.refs_0_), channel_id=1, source_target_pairs={{0,8},{1,3},{2,10},{3,1},{4,12},{5,7},{6,14},{7,5},{8,0},{9,11},{1... | collective-permute-start | bytes 442376 | tf_op jit(solution)/shard_map/ppermute | solution.py:259
  15.5 6.9 %collective-permute-start.2 = (bf16[2,9,32,128]{3,2,1,0:T(8,128)(2,1)S(1)}, bf16[2,9,32,128]{3,2,1,0:T(8,128)(2,1)S(1)}, u32[]{:S(2)}, u32[]{:S(2)}) collective-permute-start(bf16[2,9,32,128]{3,2,1,0:T(8,128)(2,1)S(1)} %shard_map.97.refs_0_), channel_id=1, source_target_pairs={{0,4},{1,9},{2,6},{3,11},{4,0},{5,13},{6,2},{7,15},{8,12},{9,1},{1... | collective-permute-start | bytes 442376 | tf_op jit(solution)/shard_map/ppermute | solution.py:259
  17.0 7.3 %collective-permute-start.1 = (bf16[2,9,32,128]{3,2,1,0:T(8,128)(2,1)S(1)}, bf16[2,9,32,128]{3,2,1,0:T(8,128)(2,1)S(1)}, u32[]{:S(2)}, u32[]{:S(2)}) collective-permute-start(bf16[2,9,32,128]{3,2,1,0:T(8,128)(2,1)S(1)} %shard_map.97.refs_0_), channel_id=1, source_target_pairs={{0,2},{1,5},{2,0},{3,7},{4,6},{5,1},{6,4},{7,3},{8,10},{9,13},{10,... | collective-permute-start | bytes 442376 | tf_op jit(solution)/shard_map/ppermute | solution.py:259
  19.1 12.6 %collective-permute-start.7 = (bf16[2,9,32,128]{3,2,1,0:T(8,128)(2,1)S(1)}, bf16[2,9,32,128]{3,2,1,0:T(8,128)(2,1)S(1)}, u32[]{:S(2)}, u32[]{:S(2)}) collective-permute-start(bf16[2,9,32,128]{3,2,1,0:T(8,128)(2,1)S(1)} %shard_map.97.refs_0_), channel_id=1, source_target_pairs={{0,14},{1,15},{2,12},{3,13},{4,10},{5,11},{6,8},{7,9},{8,6},{9,7},... | collective-permute-start | bytes 442376 | tf_op jit(solution)/shard_map/ppermute | solution.py:259
  24.4 7.9 %collective-permute-start.4 = (bf16[2,9,32,128]{3,2,1,0:T(8,128)(2,1)S(1)}, bf16[2,9,32,128]{3,2,1,0:T(8,128)(2,1)S(1)}, u32[]{:S(2)}, u32[]{:S(2)}) collective-permute-start(bf16[2,9,32,128]{3,2,1,0:T(8,128)(2,1)S(1)} %collective-permute-done.1.refs_1_), channel_id=1, source_target_pairs={{0,4},{1,9},{2,6},{3,11},{4,0},{5,13},{6,2},{7,15},{8,12},{9,1},{1... | collective-permute-start | bytes 442376 | tf_op jit(solution)/shard_map/ppermute | solution.py:259
  24.9 6.9 %collective-permute-start.8 = (bf16[1,32,256]{2,1,0:T(8,128)(2,1)S(1)}, bf16[1,32,256]{2,1,0:T(8,128)(2,1)S(1)}, u32[]{:S(2)}, u32[]{:S(2)}) collective-permute-start(bf16[1,32,256]{2,1,0:T(8,128)(2,1)S(1)} %copy-done.12), channel_id=1, source_target_pairs={{1,3},{3,5},{5,7},{7,9},{9,11},{11,13},{13,15},{15,17},{17,19},{19... | collective-permute-start | bytes 49160 | tf_op jit(solution)/shard_map/ppermute | solution.py:392
  26.1 8.8 %collective-permute-start.6 = (bf16[2,9,32,128]{3,2,1,0:T(8,128)(2,1)S(1)}, bf16[2,9,32,128]{3,2,1,0:T(8,128)(2,1)S(1)}, u32[]{:S(2)}, u32[]{:S(2)}) collective-permute-start(bf16[2,9,32,128]{3,2,1,0:T(8,128)(2,1)S(1)} %collective-permute-done.2.refs_2_), channel_id=1, source_target_pairs={{0,8},{1,3},{2,10},{3,1},{4,12},{5,7},{6,14},{7,5},{8,0},{9,11},{1... | collective-permute-start | bytes 442376 | tf_op jit(solution)/shard_map/ppermute | solution.py:259
  31.7 5.1 %collective-permute-start.5 = (bf16[2,9,32,128]{3,2,1,0:T(8,128)(2,1)S(1)}, bf16[2,9,32,128]{3,2,1,0:T(8,128)(2,1)S(1)}, u32[]{:S(2)}, u32[]{:S(2)}) collective-permute-start(bf16[2,9,32,128]{3,2,1,0:T(8,128)(2,1)S(1)} %collective-permute-done.3.refs_4_), channel_id=1, source_target_pairs={{0,2},{1,5},{2,0},{3,7},{4,6},{5,1},{6,4},{7,3},{8,10},{9,13},{10,... | collective-permute-start | bytes 442376 | tf_op jit(solution)/shard_map/ppermute | solution.py:259
  31.7 5.1 %collective-permute-start.9 = (bf16[2,9,32,128]{3,2,1,0:T(8,128)(2,1)S(1)}, bf16[2,9,32,128]{3,2,1,0:T(8,128)(2,1)S(1)}, u32[]{:S(2)}, u32[]{:S(2)}) collective-permute-start(bf16[2,9,32,128]{3,2,1,0:T(8,128)(2,1)S(1)} %shard_map.97.refs_0_), channel_id=1, source_target_pairs={{0,1},{1,0},{2,3},{3,2},{4,5},{5,4},{6,7},{7,6},{8,9},{9,8},{10,11... | collective-permute-start | bytes 442376 | tf_op jit(solution)/shard_map/ppermute | solution.py:264
  31.8 5.6 %collective-permute-start.10 = (bf16[2,9,32,128]{3,2,1,0:T(8,128)(2,1)S(1)}, bf16[2,9,32,128]{3,2,1,0:T(8,128)(2,1)S(1)}, u32[]{:S(2)}, u32[]{:S(2)}) collective-permute-start(bf16[2,9,32,128]{3,2,1,0:T(8,128)(2,1)S(1)} %collective-permute-done.1.refs_1_), channel_id=1, source_target_pairs={{0,1},{1,0},{2,3},{3,2},{4,5},{5,4},{6,7},{7,6},{8,9},{9,8},{10,11... | collective-permute-start | bytes 442376 | tf_op jit(solution)/shard_map/ppermute | solution.py:264
  32.3 5.2 %collective-permute-start.11 = (bf16[2,9,32,128]{3,2,1,0:T(8,128)(2,1)S(1)}, bf16[2,9,32,128]{3,2,1,0:T(8,128)(2,1)S(1)}, u32[]{:S(2)}, u32[]{:S(2)}) collective-permute-start(bf16[2,9,32,128]{3,2,1,0:T(8,128)(2,1)S(1)} %collective-permute-done.2.refs_2_), channel_id=1, source_target_pairs={{0,1},{1,0},{2,3},{3,2},{4,5},{5,4},{6,7},{7,6},{8,9},{9,8},{10,11... | collective-permute-start | bytes 442376 | tf_op jit(solution)/shard_map/ppermute | solution.py:264
  34.9 3.0 %collective-permute-start.13 = (bf16[2,9,32,128]{3,2,1,0:T(8,128)(2,1)S(1)}, bf16[2,9,32,128]{3,2,1,0:T(8,128)(2,1)S(1)}, u32[]{:S(2)}, u32[]{:S(2)}) collective-permute-start(bf16[2,9,32,128]{3,2,1,0:T(8,128)(2,1)S(1)} %collective-permute-done.3.refs_4_), channel_id=1, source_target_pairs={{0,1},{1,0},{2,3},{3,2},{4,5},{5,4},{6,7},{7,6},{8,9},{9,8},{10,11... | collective-permute-start | bytes 442376 | tf_op jit(solution)/shard_map/ppermute | solution.py:264
  36.9 1.4 %collective-permute-start.12 = (bf16[2,9,32,128]{3,2,1,0:T(8,128)(2,1)S(1)}, bf16[2,9,32,128]{3,2,1,0:T(8,128)(2,1)S(1)}, u32[]{:S(2)}, u32[]{:S(2)}) collective-permute-start(bf16[2,9,32,128]{3,2,1,0:T(8,128)(2,1)S(1)} %collective-permute-done.4.refs_3_), channel_id=1, source_target_pairs={{0,1},{1,0},{2,3},{3,2},{4,5},{5,4},{6,7},{7,6},{8,9},{9,8},{10,11... | collective-permute-start | bytes 442376 | tf_op jit(solution)/shard_map/ppermute | solution.py:264
  36.9 1.6 %collective-permute-start.14 = (bf16[2,9,32,128]{3,2,1,0:T(8,128)(2,1)S(1)}, bf16[2,9,32,128]{3,2,1,0:T(8,128)(2,1)S(1)}, u32[]{:S(2)}, u32[]{:S(2)}) collective-permute-start(bf16[2,9,32,128]{3,2,1,0:T(8,128)(2,1)S(1)} %collective-permute-done.5.refs_5_), channel_id=1, source_target_pairs={{0,1},{1,0},{2,3},{3,2},{4,5},{5,4},{6,7},{7,6},{8,9},{9,8},{10,11... | collective-permute-start | bytes 442376 | tf_op jit(solution)/shard_map/ppermute | solution.py:264
  37.4 1.4 %collective-permute-start.15 = (bf16[2,9,32,128]{3,2,1,0:T(8,128)(2,1)S(1)}, bf16[2,9,32,128]{3,2,1,0:T(8,128)(2,1)S(1)}, u32[]{:S(2)}, u32[]{:S(2)}) collective-permute-start(bf16[2,9,32,128]{3,2,1,0:T(8,128)(2,1)S(1)} %collective-permute-done.6.refs_6_), channel_id=1, source_target_pairs={{0,1},{1,0},{2,3},{3,2},{4,5},{5,4},{6,7},{7,6},{8,9},{9,8},{10,11... | collective-permute-start | bytes 442376 | tf_op jit(solution)/shard_map/ppermute | solution.py:264
  37.5 1.5 %collective-permute-start.16 = (bf16[2,9,32,128]{3,2,1,0:T(8,128)(2,1)S(1)}, bf16[2,9,32,128]{3,2,1,0:T(8,128)(2,1)S(1)}, u32[]{:S(2)}, u32[]{:S(2)}) collective-permute-start(bf16[2,9,32,128]{3,2,1,0:T(8,128)(2,1)S(1)} %collective-permute-done.7.refs_7_), channel_id=1, source_target_pairs={{0,1},{1,0},{2,3},{3,2},{4,5},{5,4},{6,7},{7,6},{8,9},{9,8},{10,11... | collective-permute-start | bytes 442376 | tf_op jit(solution)/shard_map/ppermute | solution.py:264
  39.0 18.9 %copy-start.11 = (bf16[1,32,256]{2,1,0:T(8,128)(2,1)S(1)}, bf16[1,32,256]{2,1,0:T(8,128)(2,1)}, u32[]{:S(2)}) copy-start(bf16[1,32,256]{2,1,0:T(8,128)(2,1)} %get-tuple-element.153) | copy-start | bytes 49156
  42.6 2.1 %collective-permute-start.17 = (bf16[4,2,9,32,128]{4,3,2,1,0:T(8,128)(2,1)S(1)}, bf16[4,2,9,32,128]{4,3,2,1,0:T(8,128)(2,1)S(1)}, u32[]{:S(2)}, u32[]{:S(2)}) collective-permute-start(bf16[4,2,9,32,128]{4,3,2,1,0:T(8,128)(2,1)S(1)} %get-tuple-element.128), channel_id=1, source_target_pairs={{0,1},{1,0},{2,3},{3,2},{4,5},{5,4},{6,7},{7,6},{8,9},{9,8},{10,11... | collective-permute-start | bytes 1769480 | tf_op jit(solution)/shard_map/ppermute | solution.py:264
  44.8 9.7 %collective-permute-start.21 = (bf16[4,2,9,32,128]{4,3,2,1,0:T(8,128)(2,1)S(1)}, bf16[4,2,9,32,128]{4,3,2,1,0:T(8,128)(2,1)S(1)}, u32[]{:S(2)}, u32[]{:S(2)}) collective-permute-start(bf16[4,2,9,32,128]{4,3,2,1,0:T(8,128)(2,1)S(1)} %get-tuple-element.137), channel_id=1, source_target_pairs={{0,1},{1,0},{2,3},{3,2},{4,5},{5,4},{6,7},{7,6},{8,9},{9,8},{10,11... | collective-permute-start | bytes 1769480 | tf_op jit(solution)/shard_map/ppermute | solution.py:264
  45.2 6.9 %collective-permute-start.18 = (bf16[2,9,32,128]{3,2,1,0:T(8,128)(2,1)S(1)}, bf16[2,9,32,128]{3,2,1,0:T(8,128)(2,1)S(1)}, u32[]{:S(2)}, u32[]{:S(2)}) collective-permute-start(bf16[2,9,32,128]{3,2,1,0:T(8,128)(2,1)S(1)} %get-tuple-element.134), channel_id=1, source_target_pairs={{0,4},{1,9},{2,6},{3,11},{4,0},{5,13},{6,2},{7,15},{8,12},{9,1},{1... | collective-permute-start | bytes 442376 | tf_op jit(solution)/shard_map/ppermute | solution.py:259
  45.2 6.9 %collective-permute-start.19 = (bf16[2,9,32,128]{3,2,1,0:T(8,128)(2,1)S(1)}, bf16[2,9,32,128]{3,2,1,0:T(8,128)(2,1)S(1)}, u32[]{:S(2)}, u32[]{:S(2)}) collective-permute-start(bf16[2,9,32,128]{3,2,1,0:T(8,128)(2,1)S(1)} %get-tuple-element.135), channel_id=1, source_target_pairs={{0,8},{1,3},{2,10},{3,1},{4,12},{5,7},{6,14},{7,5},{8,0},{9,11},{1... | collective-permute-start | bytes 442376 | tf_op jit(solution)/shard_map/ppermute | solution.py:259
  46.2 8.3 %collective-permute-start.20 = (bf16[2,9,32,128]{3,2,1,0:T(8,128)(2,1)S(1)}, bf16[2,9,32,128]{3,2,1,0:T(8,128)(2,1)S(1)}, u32[]{:S(2)}, u32[]{:S(2)}) collective-permute-start(bf16[2,9,32,128]{3,2,1,0:T(8,128)(2,1)S(1)} %get-tuple-element.136), channel_id=1, source_target_pairs={{0,2},{1,5},{2,0},{3,7},{4,6},{5,1},{6,4},{7,3},{8,10},{9,13},{10,... | collective-permute-start | bytes 442376 | tf_op jit(solution)/shard_map/ppermute | solution.py:259
  46.3 14.0 %collective-permute-start.25 = (bf16[2,9,32,128]{3,2,1,0:T(8,128)(2,1)S(1)}, bf16[2,9,32,128]{3,2,1,0:T(8,128)(2,1)S(1)}, u32[]{:S(2)}, u32[]{:S(2)}) collective-permute-start(bf16[2,9,32,128]{3,2,1,0:T(8,128)(2,1)S(1)} %get-tuple-element.152), channel_id=1, source_target_pairs={{0,14},{1,15},{2,12},{3,13},{4,10},{5,11},{6,8},{7,9},{8,6},{9,7},... | collective-permute-start | bytes 442376 | tf_op jit(solution)/shard_map/ppermute | solution.py:259
  54.8 6.5 %collective-permute-start.22 = (bf16[2,9,32,128]{3,2,1,0:T(8,128)(2,1)S(1)}, bf16[2,9,32,128]{3,2,1,0:T(8,128)(2,1)S(1)}, u32[]{:S(2)}, u32[]{:S(2)}) collective-permute-start(bf16[2,9,32,128]{3,2,1,0:T(8,128)(2,1)S(1)} %get-tuple-element.149), channel_id=1, source_target_pairs={{0,2},{1,5},{2,0},{3,7},{4,6},{5,1},{6,4},{7,3},{8,10},{9,13},{10,... | collective-permute-start | bytes 442376 | tf_op jit(solution)/shard_map/ppermute | solution.py:259
  54.8 6.4 %collective-permute-start.23 = (bf16[2,9,32,128]{3,2,1,0:T(8,128)(2,1)S(1)}, bf16[2,9,32,128]{3,2,1,0:T(8,128)(2,1)S(1)}, u32[]{:S(2)}, u32[]{:S(2)}) collective-permute-start(bf16[2,9,32,128]{3,2,1,0:T(8,128)(2,1)S(1)} %get-tuple-element.150), channel_id=1, source_target_pairs={{0,4},{1,9},{2,6},{3,11},{4,0},{5,13},{6,2},{7,15},{8,12},{9,1},{1... | collective-permute-start | bytes 442376 | tf_op jit(solution)/shard_map/ppermute | solution.py:259
  56.0 5.2 %collective-permute-start.24 = (bf16[2,9,32,128]{3,2,1,0:T(8,128)(2,1)S(1)}, bf16[2,9,32,128]{3,2,1,0:T(8,128)(2,1)S(1)}, u32[]{:S(2)}, u32[]{:S(2)}) collective-permute-start(bf16[2,9,32,128]{3,2,1,0:T(8,128)(2,1)S(1)} %get-tuple-element.151), channel_id=1, source_target_pairs={{0,8},{1,3},{2,10},{3,1},{4,12},{5,7},{6,14},{7,5},{8,0},{9,11},{1... | collective-permute-start | bytes 442376 | tf_op jit(solution)/shard_map/ppermute | solution.py:259
  57.8 1.2 collective-permute-start.26
  59.0 1.2 collective-permute-start.27
  61.3 5.3 %collective-permute-start.28 = (bf16[9,32,128]{2,1,0:T(8,128)(2,1)S(1)}, bf16[9,32,128]{2,1,0:T(8,128)(2,1)S(1)}, u32[]{:S(2)}, u32[]{:S(2)}) collective-permute-start(bf16[9,32,128]{2,1,0:T(8,128)(2,1)S(1)} %get-tuple-element.162), channel_id=1, source_target_pairs={{0,16},{1,17},{2,18},{3,19},{4,20},{5,21},{6,22},{7,23},{8,24},{9,... | collective-permute-start | bytes 221192 | tf_op jit(solution)/shard_map/ppermute | solution.py:255
  68.3 5.3 %collective-permute-start.29 = (bf16[9,32,128]{2,1,0:T(8,128)(2,1)S(1)}, bf16[9,32,128]{2,1,0:T(8,128)(2,1)S(1)}, u32[]{:S(2)}, u32[]{:S(2)}) collective-permute-start(bf16[9,32,128]{2,1,0:T(8,128)(2,1)S(1)} %get-tuple-element.164.refs_0_), channel_id=1, source_target_pairs={{0,16},{1,17},{2,18},{3,19},{4,20},{5,21},{6,22},{7,23},{8,24},{9,... | collective-permute-start | bytes 221192 | tf_op jit(solution)/shard_map/ppermute | solution.py:255
  73.5 8.0 %collective-permute-start.32 = (bf16[2,9,32,128]{3,2,1,0:T(8,128)(2,1)S(1)}, bf16[2,9,32,128]{3,2,1,0:T(8,128)(2,1)S(1)}, u32[]{:S(2)}, u32[]{:S(2)}) collective-permute-start(bf16[2,9,32,128]{3,2,1,0:T(8,128)(2,1)S(1)} %shard_map.106.refs_0_), channel_id=1, source_target_pairs={{0,8},{1,3},{2,10},{3,1},{4,12},{5,7},{6,14},{7,5},{8,0},{9,11},{1... | collective-permute-start | bytes 442376 | tf_op jit(solution)/shard_map/ppermute | solution.py:259
  75.3 6.3 %collective-permute-start.31 = (bf16[2,9,32,128]{3,2,1,0:T(8,128)(2,1)S(1)}, bf16[2,9,32,128]{3,2,1,0:T(8,128)(2,1)S(1)}, u32[]{:S(2)}, u32[]{:S(2)}) collective-permute-start(bf16[2,9,32,128]{3,2,1,0:T(8,128)(2,1)S(1)} %shard_map.106.refs_0_), channel_id=1, source_target_pairs={{0,4},{1,9},{2,6},{3,11},{4,0},{5,13},{6,2},{7,15},{8,12},{9,1},{1... | collective-permute-start | bytes 442376 | tf_op jit(solution)/shard_map/ppermute | solution.py:259
  76.3 5.8 %collective-permute-start.30 = (bf16[2,9,32,128]{3,2,1,0:T(8,128)(2,1)S(1)}, bf16[2,9,32,128]{3,2,1,0:T(8,128)(2,1)S(1)}, u32[]{:S(2)}, u32[]{:S(2)}) collective-permute-start(bf16[2,9,32,128]{3,2,1,0:T(8,128)(2,1)S(1)} %shard_map.106.refs_0_), channel_id=1, source_target_pairs={{0,2},{1,5},{2,0},{3,7},{4,6},{5,1},{6,4},{7,3},{8,10},{9,13},{10,... | collective-permute-start | bytes 442376 | tf_op jit(solution)/shard_map/ppermute | solution.py:259
  79.4 9.9 %collective-permute-start.36 = (bf16[2,9,32,128]{3,2,1,0:T(8,128)(2,1)S(1)}, bf16[2,9,32,128]{3,2,1,0:T(8,128)(2,1)S(1)}, u32[]{:S(2)}, u32[]{:S(2)}) collective-permute-start(bf16[2,9,32,128]{3,2,1,0:T(8,128)(2,1)S(1)} %shard_map.106.refs_0_), channel_id=1, source_target_pairs={{0,14},{1,15},{2,12},{3,13},{4,10},{5,11},{6,8},{7,9},{8,6},{9,7},... | collective-permute-start | bytes 442376 | tf_op jit(solution)/shard_map/ppermute | solution.py:259
  82.2 7.6 %collective-permute-start.33 = (bf16[2,9,32,128]{3,2,1,0:T(8,128)(2,1)S(1)}, bf16[2,9,32,128]{3,2,1,0:T(8,128)(2,1)S(1)}, u32[]{:S(2)}, u32[]{:S(2)}) collective-permute-start(bf16[2,9,32,128]{3,2,1,0:T(8,128)(2,1)S(1)} %collective-permute-done.30.refs_1_), channel_id=1, source_target_pairs={{0,4},{1,9},{2,6},{3,11},{4,0},{5,13},{6,2},{7,15},{8,12},{9,1},{1... | collective-permute-start | bytes 442376 | tf_op jit(solution)/shard_map/ppermute | solution.py:259
  83.5 5.8 %collective-permute-start.37 = (bf16[1,32,256]{2,1,0:T(8,128)(2,1)S(1)}, bf16[1,32,256]{2,1,0:T(8,128)(2,1)S(1)}, u32[]{:S(2)}, u32[]{:S(2)}) collective-permute-start(bf16[1,32,256]{2,1,0:T(8,128)(2,1)S(1)} %get-tuple-element.170), channel_id=1, source_target_pairs={{1,3},{3,5},{5,7},{7,9},{9,11},{11,13},{13,15},{15,17},{17,19},{19... | collective-permute-start | bytes 49160 | tf_op jit(solution)/shard_map/ppermute | solution.py:392
  84.8 7.1 %collective-permute-start.35 = (bf16[2,9,32,128]{3,2,1,0:T(8,128)(2,1)S(1)}, bf16[2,9,32,128]{3,2,1,0:T(8,128)(2,1)S(1)}, u32[]{:S(2)}, u32[]{:S(2)}) collective-permute-start(bf16[2,9,32,128]{3,2,1,0:T(8,128)(2,1)S(1)} %collective-permute-done.31.refs_2_), channel_id=1, source_target_pairs={{0,8},{1,3},{2,10},{3,1},{4,12},{5,7},{6,14},{7,5},{8,0},{9,11},{1... | collective-permute-start | bytes 442376 | tf_op jit(solution)/shard_map/ppermute | solution.py:259
  88.7 5.1 %collective-permute-start.34 = (bf16[2,9,32,128]{3,2,1,0:T(8,128)(2,1)S(1)}, bf16[2,9,32,128]{3,2,1,0:T(8,128)(2,1)S(1)}, u32[]{:S(2)}, u32[]{:S(2)}) collective-permute-start(bf16[2,9,32,128]{3,2,1,0:T(8,128)(2,1)S(1)} %collective-permute-done.32.refs_4_), channel_id=1, source_target_pairs={{0,2},{1,5},{2,0},{3,7},{4,6},{5,1},{6,4},{7,3},{8,10},{9,13},{10,... | collective-permute-start | bytes 442376 | tf_op jit(solution)/shard_map/ppermute | solution.py:259
  89.3 4.6 %collective-permute-start.38 = (bf16[2,9,32,128]{3,2,1,0:T(8,128)(2,1)S(1)}, bf16[2,9,32,128]{3,2,1,0:T(8,128)(2,1)S(1)}, u32[]{:S(2)}, u32[]{:S(2)}) collective-permute-start(bf16[2,9,32,128]{3,2,1,0:T(8,128)(2,1)S(1)} %shard_map.106.refs_0_), channel_id=1, source_target_pairs={{0,1},{1,0},{2,3},{3,2},{4,5},{5,4},{6,7},{7,6},{8,9},{9,8},{10,11... | collective-permute-start | bytes 442376 | tf_op jit(solution)/shard_map/ppermute | solution.py:264
  89.3 5.1 %collective-permute-start.39 = (bf16[2,9,32,128]{3,2,1,0:T(8,128)(2,1)S(1)}, bf16[2,9,32,128]{3,2,1,0:T(8,128)(2,1)S(1)}, u32[]{:S(2)}, u32[]{:S(2)}) collective-permute-start(bf16[2,9,32,128]{3,2,1,0:T(8,128)(2,1)S(1)} %collective-permute-done.30.refs_1_), channel_id=1, source_target_pairs={{0,1},{1,0},{2,3},{3,2},{4,5},{5,4},{6,7},{7,6},{8,9},{9,8},{10,11... | collective-permute-start | bytes 442376 | tf_op jit(solution)/shard_map/ppermute | solution.py:264
  89.8 4.6 %collective-permute-start.40 = (bf16[2,9,32,128]{3,2,1,0:T(8,128)(2,1)S(1)}, bf16[2,9,32,128]{3,2,1,0:T(8,128)(2,1)S(1)}, u32[]{:S(2)}, u32[]{:S(2)}) collective-permute-start(bf16[2,9,32,128]{3,2,1,0:T(8,128)(2,1)S(1)} %collective-permute-done.31.refs_2_), channel_id=1, source_target_pairs={{0,1},{1,0},{2,3},{3,2},{4,5},{5,4},{6,7},{7,6},{8,9},{9,8},{10,11... | collective-permute-start | bytes 442376 | tf_op jit(solution)/shard_map/ppermute | solution.py:264
  91.9 3.0 %collective-permute-start.42 = (bf16[2,9,32,128]{3,2,1,0:T(8,128)(2,1)S(1)}, bf16[2,9,32,128]{3,2,1,0:T(8,128)(2,1)S(1)}, u32[]{:S(2)}, u32[]{:S(2)}) collective-permute-start(bf16[2,9,32,128]{3,2,1,0:T(8,128)(2,1)S(1)} %collective-permute-done.32.refs_4_), channel_id=1, source_target_pairs={{0,1},{1,0},{2,3},{3,2},{4,5},{5,4},{6,7},{7,6},{8,9},{9,8},{10,11... | collective-permute-start | bytes 442376 | tf_op jit(solution)/shard_map/ppermute | solution.py:264
  93.9 1.4 %collective-permute-start.41 = (bf16[2,9,32,128]{3,2,1,0:T(8,128)(2,1)S(1)}, bf16[2,9,32,128]{3,2,1,0:T(8,128)(2,1)S(1)}, u32[]{:S(2)}, u32[]{:S(2)}) collective-permute-start(bf16[2,9,32,128]{3,2,1,0:T(8,128)(2,1)S(1)} %collective-permute-done.33.refs_3_), channel_id=1, source_target_pairs={{0,1},{1,0},{2,3},{3,2},{4,5},{5,4},{6,7},{7,6},{8,9},{9,8},{10,11... | collective-permute-start | bytes 442376 | tf_op jit(solution)/shard_map/ppermute | solution.py:264
  93.9 1.6 %collective-permute-start.43 = (bf16[2,9,32,128]{3,2,1,0:T(8,128)(2,1)S(1)}, bf16[2,9,32,128]{3,2,1,0:T(8,128)(2,1)S(1)}, u32[]{:S(2)}, u32[]{:S(2)}) collective-permute-start(bf16[2,9,32,128]{3,2,1,0:T(8,128)(2,1)S(1)} %collective-permute-done.34.refs_5_), channel_id=1, source_target_pairs={{0,1},{1,0},{2,3},{3,2},{4,5},{5,4},{6,7},{7,6},{8,9},{9,8},{10,11... | collective-permute-start | bytes 442376 | tf_op jit(solution)/shard_map/ppermute | solution.py:264
  94.4 1.4 %collective-permute-start.44 = (bf16[2,9,32,128]{3,2,1,0:T(8,128)(2,1)S(1)}, bf16[2,9,32,128]{3,2,1,0:T(8,128)(2,1)S(1)}, u32[]{:S(2)}, u32[]{:S(2)}) collective-permute-start(bf16[2,9,32,128]{3,2,1,0:T(8,128)(2,1)S(1)} %collective-permute-done.35.refs_6_), channel_id=1, source_target_pairs={{0,1},{1,0},{2,3},{3,2},{4,5},{5,4},{6,7},{7,6},{8,9},{9,8},{10,11... | collective-permute-start | bytes 442376 | tf_op jit(solution)/shard_map/ppermute | solution.py:264
  94.4 1.5 %collective-permute-start.45 = (bf16[2,9,32,128]{3,2,1,0:T(8,128)(2,1)S(1)}, bf16[2,9,32,128]{3,2,1,0:T(8,128)(2,1)S(1)}, u32[]{:S(2)}, u32[]{:S(2)}) collective-permute-start(bf16[2,9,32,128]{3,2,1,0:T(8,128)(2,1)S(1)} %collective-permute-done.36.refs_7_), channel_id=1, source_target_pairs={{0,1},{1,0},{2,3},{3,2},{4,5},{5,4},{6,7},{7,6},{8,9},{9,8},{10,11... | collective-permute-start | bytes 442376 | tf_op jit(solution)/shard_map/ppermute | solution.py:264
  99.6 2.1 %collective-permute-start.46 = (bf16[4,2,9,32,128]{4,3,2,1,0:T(8,128)(2,1)S(1)}, bf16[4,2,9,32,128]{4,3,2,1,0:T(8,128)(2,1)S(1)}, u32[]{:S(2)}, u32[]{:S(2)}) collective-permute-start(bf16[4,2,9,32,128]{4,3,2,1,0:T(8,128)(2,1)S(1)} %get-tuple-element.181), channel_id=1, source_target_pairs={{0,1},{1,0},{2,3},{3,2},{4,5},{5,4},{6,7},{7,6},{8,9},{9,8},{10,11... | collective-permute-start | bytes 1769480 | tf_op jit(solution)/shard_map/ppermute | solution.py:264
  101.8 10.5 %collective-permute-start.50 = (bf16[4,2,9,32,128]{4,3,2,1,0:T(8,128)(2,1)S(1)}, bf16[4,2,9,32,128]{4,3,2,1,0:T(8,128)(2,1)S(1)}, u32[]{:S(2)}, u32[]{:S(2)}) collective-permute-start(bf16[4,2,9,32,128]{4,3,2,1,0:T(8,128)(2,1)S(1)} %get-tuple-element.190), channel_id=1, source_target_pairs={{0,1},{1,0},{2,3},{3,2},{4,5},{5,4},{6,7},{7,6},{8,9},{9,8},{10,11... | collective-permute-start | bytes 1769480 | tf_op jit(solution)/shard_map/ppermute | solution.py:264
  102.1 6.4 %collective-permute-start.47 = (bf16[2,9,32,128]{3,2,1,0:T(8,128)(2,1)S(1)}, bf16[2,9,32,128]{3,2,1,0:T(8,128)(2,1)S(1)}, u32[]{:S(2)}, u32[]{:S(2)}) collective-permute-start(bf16[2,9,32,128]{3,2,1,0:T(8,128)(2,1)S(1)} %get-tuple-element.187), channel_id=1, source_target_pairs={{0,4},{1,9},{2,6},{3,11},{4,0},{5,13},{6,2},{7,15},{8,12},{9,1},{1... | collective-permute-start | bytes 442376 | tf_op jit(solution)/shard_map/ppermute | solution.py:259
  103.4 6.5 %collective-permute-start.48 = (bf16[2,9,32,128]{3,2,1,0:T(8,128)(2,1)S(1)}, bf16[2,9,32,128]{3,2,1,0:T(8,128)(2,1)S(1)}, u32[]{:S(2)}, u32[]{:S(2)}) collective-permute-start(bf16[2,9,32,128]{3,2,1,0:T(8,128)(2,1)S(1)} %get-tuple-element.188), channel_id=1, source_target_pairs={{0,8},{1,3},{2,10},{3,1},{4,12},{5,7},{6,14},{7,5},{8,0},{9,11},{1... | collective-permute-start | bytes 442376 | tf_op jit(solution)/shard_map/ppermute | solution.py:259
  104.2 8.2 %collective-permute-start.49 = (bf16[2,9,32,128]{3,2,1,0:T(8,128)(2,1)S(1)}, bf16[2,9,32,128]{3,2,1,0:T(8,128)(2,1)S(1)}, u32[]{:S(2)}, u32[]{:S(2)}) collective-permute-start(bf16[2,9,32,128]{3,2,1,0:T(8,128)(2,1)S(1)} %get-tuple-element.189), channel_id=1, source_target_pairs={{0,2},{1,5},{2,0},{3,7},{4,6},{5,1},{6,4},{7,3},{8,10},{9,13},{10,... | collective-permute-start | bytes 442376 | tf_op jit(solution)/shard_map/ppermute | solution.py:259
  104.7 13.1 %collective-permute-start.54 = (bf16[2,9,32,128]{3,2,1,0:T(8,128)(2,1)S(1)}, bf16[2,9,32,128]{3,2,1,0:T(8,128)(2,1)S(1)}, u32[]{:S(2)}, u32[]{:S(2)}) collective-permute-start(bf16[2,9,32,128]{3,2,1,0:T(8,128)(2,1)S(1)} %get-tuple-element.205), channel_id=1, source_target_pairs={{0,14},{1,15},{2,12},{3,13},{4,10},{5,11},{6,8},{7,9},{8,6},{9,7},... | collective-permute-start | bytes 442376 | tf_op jit(solution)/shard_map/ppermute | solution.py:259
  112.5 6.5 %collective-permute-start.51 = (bf16[2,9,32,128]{3,2,1,0:T(8,128)(2,1)S(1)}, bf16[2,9,32,128]{3,2,1,0:T(8,128)(2,1)S(1)}, u32[]{:S(2)}, u32[]{:S(2)}) collective-permute-start(bf16[2,9,32,128]{3,2,1,0:T(8,128)(2,1)S(1)} %get-tuple-element.202), channel_id=1, source_target_pairs={{0,2},{1,5},{2,0},{3,7},{4,6},{5,1},{6,4},{7,3},{8,10},{9,13},{10,... | collective-permute-start | bytes 442376 | tf_op jit(solution)/shard_map/ppermute | solution.py:259
  112.6 6.4 %collective-permute-start.52 = (bf16[2,9,32,128]{3,2,1,0:T(8,128)(2,1)S(1)}, bf16[2,9,32,128]{3,2,1,0:T(8,128)(2,1)S(1)}, u32[]{:S(2)}, u32[]{:S(2)}) collective-permute-start(bf16[2,9,32,128]{3,2,1,0:T(8,128)(2,1)S(1)} %get-tuple-element.203), channel_id=1, source_target_pairs={{0,4},{1,9},{2,6},{3,11},{4,0},{5,13},{6,2},{7,15},{8,12},{9,1},{1... | collective-permute-start | bytes 442376 | tf_op jit(solution)/shard_map/ppermute | solution.py:259
  113.4 5.7 %collective-permute-start.53 = (bf16[2,9,32,128]{3,2,1,0:T(8,128)(2,1)S(1)}, bf16[2,9,32,128]{3,2,1,0:T(8,128)(2,1)S(1)}, u32[]{:S(2)}, u32[]{:S(2)}) collective-permute-start(bf16[2,9,32,128]{3,2,1,0:T(8,128)(2,1)S(1)} %get-tuple-element.204), channel_id=1, source_target_pairs={{0,8},{1,3},{2,10},{3,1},{4,12},{5,7},{6,14},{7,5},{8,0},{9,11},{1... | collective-permute-start | bytes 442376 | tf_op jit(solution)/shard_map/ppermute | solution.py:259
  115.4 1.2 collective-permute-start.55
  116.5 1.2 collective-permute-start.56
  119.1 7.3 %collective-permute-start.57 = (bf16[9,32,128]{2,1,0:T(8,128)(2,1)S(1)}, bf16[9,32,128]{2,1,0:T(8,128)(2,1)S(1)}, u32[]{:S(2)}, u32[]{:S(2)}) collective-permute-start(bf16[9,32,128]{2,1,0:T(8,128)(2,1)S(1)} %get-tuple-element.215), channel_id=1, source_target_pairs={{0,16},{1,17},{2,18},{3,19},{4,20},{5,21},{6,22},{7,23},{8,24},{9,... | collective-permute-start | bytes 221192 | tf_op jit(solution)/shard_map/ppermute | solution.py:255
  (7 other events, 59.4 us)

commit v19 on v18

--- a/solution.py
+++ b/solution.py
@@ -172,7 +172,9 @@
     own_out[...] = keep_ref[0].astype(F32) + swap_ref[0].astype(F32)
     for n, out_ref in enumerate(out_refs):
         total = keep_ref[n + 1].astype(F32) + swap_ref[n + 1].astype(F32)
-        out_ref[...] = (total + part_refs[n][...].astype(F32)).astype(BF)
+        for part_ref in part_refs[n :: len(out_refs)]:
+            total = total + part_ref[...].astype(F32)
+        out_ref[...] = total.astype(BF)
 
 
 def rows_kernel(source_ref, target_ref, source_out, target_out, *, clusters, far, magic, shift):
@@ -363,9 +365,9 @@
         compiler_params=params(16),
     )
     far_add = adder(add_kernel, 2, [part_shape] * 4)
-    middle_add = adder(functools.partial(middle_add_kernel, parts=3), 5, [own_shape] + [part_shape] * 3)
+    middle_add = adder(functools.partial(middle_add_kernel, parts=4), 6, [own_shape] + [part_shape] * 3)
     last_add = adder(
-        functools.partial(last_add_kernel, parts=4), 5, [shape(tile_shape, F32)] + [tile_out] * (far - 1)
+        functools.partial(last_add_kernel, parts=3), 4, [shape(tile_shape, F32)] + [tile_out] * (far - 1)
     )
 
     def finish(with_coeffs):
@@ -402,14 +404,15 @@
         keep_long, keep, send_long, send = totals
         corner, xy, yz, zx = far_add(keep_long, swap_cores(send_long))
         corner, xy, yz, zx, send = barrier((corner, xy, yz, zx, send))
-        to_x, to_y, to_z, swapped = barrier((swap(xy, y), swap(yz, z), swap(zx, x), swap_cores(send)))
+        to_x, to_y, to_z, corner, swapped = barrier(
+            (swap(xy, y), swap(yz, z), swap(zx, x), swap(corner, y | z), swap_cores(send))
+        )
         own, to_x, to_y, to_z, inner, outer = barrier(
-            (*middle_add(keep, swapped, to_x, to_y, to_z), inner, outer)
+            (*middle_add(keep, swapped, to_x, to_y, to_z, corner), inner, outer)
         )
         edges = edge(swap_cores(inner), swap_cores(outer), near_field, near_field)
-        parts = [swap(to_x, x), swap(to_y, y), swap(to_z, z), swap(corner, x | y | z)]
-        own, parts, edges = barrier((own, parts, edges))
-        total, *away = last_add(own, *parts)
+        own, to_x, to_y, to_z, edges = barrier((own, swap(to_x, x), swap(to_y, y), swap(to_z, z), edges))
+        total, *away = last_add(own, to_x, to_y, to_z)
         terms = [swap_far(part, s + 1) for s, part in enumerate(away)]
         return finish(with_coeffs)(ranks, near_sum, edges, basis, transfer, total, *terms)
 

time: 128 us -> 127 us (level)
  starting transfers between devices: 57.4 us -> 50.3 us
  waiting for transfers between devices: 47 us -> 52.6 us
    ppermute x28, waiting for transfers between devices: 25.7 us -> 32.6 us  [swap(): lax.ppermute(part, 'clu', [(d, d ^ (turned if d % cores else direction) *...]
    ppermute x28, starting transfers between devices: 39.2 us -> 33.6 us  [swap(): lax.ppermute(part, 'clu', [(d, d ^ (turned if d % cores else direction) *...]
    ppermute x24, waiting for transfers between devices: 9.92 us -> 7.18 us  [swap_cores(): return lax.ppermute(part, 'clu', [(d, d ^ 1) for d in range(devices)])]
    ppermute x4, starting transfers between devices: 10.6 us -> 8.42 us  [swap_far(): lax.ppermute(part, 'clu', [(d, (d + shift * cube) % devices) for d in ran...]
  transfers between devices with their start and end apart: 58 -> 58, of which waited for: 33 -> 40; matrix products, arithmetic and copies ran while one was open for 4% -> 4% of each run, Pallas kernels for 2% -> 2%
where the time goes in v19:
time: 127 us
  waiting for transfers between devices  52.6 us (41%)
  starting transfers between devices  50.3 us (40%)
  Pallas kernels  16.2 us (13%)
  local copies, waits for them, and re-layouts  6.54 us (5%)
    ppermute x28, starting transfers between devices, swap(): lax.ppermute(part, 'clu', [(d, d ^ (turned if d % cores else direction) *...  33.6 us
    ppermute x28, waiting for transfers between devices, swap(): lax.ppermute(part, 'clu', [(d, d ^ (turned if d % cores else direction) *...  32.6 us
    ppermute x4, waiting for transfers between devices, swap_far(): lax.ppermute(part, 'clu', [(d, (d + shift * cube) % devices) for d in ran...  12.4 us
    ppermute x4, starting transfers between devices, swap_far(): lax.ppermute(part, 'clu', [(d, (d + shift * cube) % devices) for d in ran...  8.42 us
    pallas_call x2, Pallas kernels, apply_matrix(): couple(source_rows, target_rows, coupling, *[got[chip] for chip in range(...  7.2 us
    ppermute x24, waiting for transfers between devices, swap_cores(): return lax.ppermute(part, 'clu', [(d, d ^ 1) for d in range(devices)])  7.18 us
    unnamed x27, local copies, waits for them, and re-layouts  6.54 us
    ppermute x24, starting transfers between devices, swap_cores(): return lax.ppermute(part, 'clu', [(d, d ^ 1) for d in range(devices)])  5.73 us
  transfers between devices with their start and end apart: 58, of which 40 were waited for; matrix products, arithmetic and copies ran while one was open for 4% of the time, Pallas kernels for 2%

profile of v19, /device:TPU:0, one launch (start us, length us, event | category | flops | bytes accessed | tf_op | source)
XLA Modules:
  0.0 126.5 jit_solution(5204995629347122669)
XLA Ops:
  0.6 2.9 %shard_map.95 = (bf16[9,32,128]{2,1,0:T(8,128)(2,1)}, bf16[1,32,256]{2,1,0:T(8,128)(2,1)}, bf16[1,32,256]{2,1,0:T(8,128)(2,1)}) custom-call(s32[12]{0:T(128)} %ranks_ref.5, bf16[8,32,256]{2,1,0:T(8,128)(2,1)} %v_ref.1, bf16[8,96,256]{2,1,0:T(8,128)(2,1)} %basis_ref.3, bf16[8,96,96]{2,1,0:T(8,128)(2,1)} %transfer_ref.3), custom_call_target="tpu_custom_call" | custom-call | tf_op jit(solution)/shard_map/pallas_call | solution.py:289
  3.6 4.1 %collective-permute-start = (bf16[9,32,128]{2,1,0:T(8,128)(2,1)}, bf16[9,32,128]{2,1,0:T(8,128)(2,1)S(1)}, u32[]{:S(2)}, u32[]{:S(2)}) collective-permute-start(bf16[9,32,128]{2,1,0:T(8,128)(2,1)} %get-tuple-element.109.__.refs_0_), channel_id=1, source_target_pairs={{0,16},{1,17},{2,18},{3,19},{4,20},{5,21},{6,22},{7,23},{8,24},{9,... | collective-permute-start | bytes 221192 | tf_op jit(solution)/shard_map/ppermute | solution.py:257
  7.7 4.8 %copy.10._.coupling_ref = bf16[128,96,96]{2,1,0:T(8,128)(2,1)} copy(bf16[128,96,96]{0,2,1:T(8,128)(2,1)} %param.12) | data formatting | bytes 4718592 | tf_op args[4]
  12.4 0.6 shard_map.96._
  13.0 0.8 copy-done.7
  13.9 1.6 %collective-permute-start.3 = (bf16[2,9,32,128]{3,2,1,0:T(8,128)(2,1)S(1)}, bf16[2,9,32,128]{3,2,1,0:T(8,128)(2,1)S(1)}, u32[]{:S(2)}, u32[]{:S(2)}) collective-permute-start(bf16[2,9,32,128]{3,2,1,0:T(8,128)(2,1)S(1)} %shard_map.97.refs_0_), channel_id=1, source_target_pairs={{0,8},{1,3},{2,10},{3,1},{4,12},{5,7},{6,14},{7,5},{8,0},{9,11},{1... | collective-permute-start | bytes 442376 | tf_op jit(solution)/shard_map/ppermute | solution.py:261
  15.5 1.5 %collective-permute-start.2 = (bf16[2,9,32,128]{3,2,1,0:T(8,128)(2,1)S(1)}, bf16[2,9,32,128]{3,2,1,0:T(8,128)(2,1)S(1)}, u32[]{:S(2)}, u32[]{:S(2)}) collective-permute-start(bf16[2,9,32,128]{3,2,1,0:T(8,128)(2,1)S(1)} %shard_map.97.refs_0_), channel_id=1, source_target_pairs={{0,4},{1,9},{2,6},{3,11},{4,0},{5,13},{6,2},{7,15},{8,12},{9,1},{1... | collective-permute-start | bytes 442376 | tf_op jit(solution)/shard_map/ppermute | solution.py:261
  17.0 1.5 %collective-permute-start.1 = (bf16[2,9,32,128]{3,2,1,0:T(8,128)(2,1)S(1)}, bf16[2,9,32,128]{3,2,1,0:T(8,128)(2,1)S(1)}, u32[]{:S(2)}, u32[]{:S(2)}) collective-permute-start(bf16[2,9,32,128]{3,2,1,0:T(8,128)(2,1)S(1)} %shard_map.97.refs_0_), channel_id=1, source_target_pairs={{0,2},{1,5},{2,0},{3,7},{4,6},{5,1},{6,4},{7,3},{8,10},{9,13},{10,... | collective-permute-start | bytes 442376 | tf_op jit(solution)/shard_map/ppermute | solution.py:261
  18.5 0.6 shard_map.98.near_ref
  19.5 1.0 collective-permute-done.3.refs_4_
  20.5 1.9 %collective-permute-done.2.refs_2_ = bf16[2,9,32,128]{3,2,1,0:T(8,128)(2,1)S(1)} collective-permute-done((bf16[2,9,32,128]{3,2,1,0:T(8,128)(2,1)S(1)}, bf16[2,9,32,128]{3,2,1,0:T(8,128)(2,1)S(1)}, u32[]{:S(2)}, u32[]{:S(2)}) %collective-permute-start.2) | collective-permute-done | bytes 147488 | tf_op jit(solution)/shard_map/ppermute | solution.py:261
  22.4 1.9 %collective-permute-done.1.refs_1_ = bf16[2,9,32,128]{3,2,1,0:T(8,128)(2,1)S(1)} collective-permute-done((bf16[2,9,32,128]{3,2,1,0:T(8,128)(2,1)S(1)}, bf16[2,9,32,128]{3,2,1,0:T(8,128)(2,1)S(1)}, u32[]{:S(2)}, u32[]{:S(2)}) %collective-permute-start.1) | collective-permute-done | bytes 147488 | tf_op jit(solution)/shard_map/ppermute | solution.py:261
  24.9 1.3 %collective-permute-start.8 = (bf16[1,32,256]{2,1,0:T(8,128)(2,1)S(1)}, bf16[1,32,256]{2,1,0:T(8,128)(2,1)S(1)}, u32[]{:S(2)}, u32[]{:S(2)}) collective-permute-start(bf16[1,32,256]{2,1,0:T(8,128)(2,1)S(1)} %copy-done.12), channel_id=1, source_target_pairs={{1,3},{3,5},{5,7},{7,9},{9,11},{11,13},{13,15},{15,17},{17,19},{19... | collective-permute-start | bytes 49160 | tf_op jit(solution)/shard_map/ppermute | solution.py:394
  26.1 5.6 %collective-permute-start.6 = (bf16[2,9,32,128]{3,2,1,0:T(8,128)(2,1)S(1)}, bf16[2,9,32,128]{3,2,1,0:T(8,128)(2,1)S(1)}, u32[]{:S(2)}, u32[]{:S(2)}) collective-permute-start(bf16[2,9,32,128]{3,2,1,0:T(8,128)(2,1)S(1)} %collective-permute-done.2.refs_2_), channel_id=1, source_target_pairs={{0,8},{1,3},{2,10},{3,1},{4,12},{5,7},{6,14},{7,5},{8,0},{9,11},{1... | collective-permute-start | bytes 442376 | tf_op jit(solution)/shard_map/ppermute | solution.py:261
  32.3 2.6 %collective-permute-done.6.refs_6_ = bf16[2,9,32,128]{3,2,1,0:T(8,128)(2,1)S(1)} collective-permute-done((bf16[2,9,32,128]{3,2,1,0:T(8,128)(2,1)S(1)}, bf16[2,9,32,128]{3,2,1,0:T(8,128)(2,1)S(1)}, u32[]{:S(2)}, u32[]{:S(2)}) %collective-permute-start.6) | collective-permute-done | bytes 147488 | tf_op jit(solution)/shard_map/ppermute | solution.py:261
  34.9 1.9 %collective-permute-done.5.refs_5_ = bf16[2,9,32,128]{3,2,1,0:T(8,128)(2,1)S(1)} collective-permute-done((bf16[2,9,32,128]{3,2,1,0:T(8,128)(2,1)S(1)}, bf16[2,9,32,128]{3,2,1,0:T(8,128)(2,1)S(1)}, u32[]{:S(2)}, u32[]{:S(2)}) %collective-permute-start.5) | collective-permute-done | bytes 147488 | tf_op jit(solution)/shard_map/ppermute | solution.py:261
  39.0 3.6 %shard_map.100 = (bf16[4,2,9,32,128]{4,3,2,1,0:T(8,128)(2,1)S(1)}, bf16[4,2,9,32,128]{4,3,2,1,0:T(8,128)(2,1)S(1)}, bf16[4,2,9,32,128]{4,3,2,1,0:T(8,128)(2,1)S(1)}, bf16[4,2,9,32,128]{4,3,2,1,0:T(8,128)(2,1)S(1)}) custom-call(s32[128]{0:T(128)S(1)} %bitcast.4, s32[128]{0:T(128)S(1)} %bitcast.6, bf16[128,96,96]{2,1,0:T(8,128)(2,1)S(1)} %copy-done.1, ...), custom_call_target="tpu_custom_call" | custom-call | flops 75497472 | bytes 10485760 | tf_op jit(solution)/shard_map/pallas_call | solution.py:397
  43.0 1.7 %collective-permute-done.17.swap_ref = bf16[4,2,9,32,128]{4,3,2,1,0:T(8,128)(2,1)S(1)} collective-permute-done((bf16[4,2,9,32,128]{4,3,2,1,0:T(8,128)(2,1)S(1)}, bf16[4,2,9,32,128]{4,3,2,1,0:T(8,128)(2,1)S(1)}, u32[]{:S(2)}, u32[]{:S(2)}) %collective-permute-start.17) | collective-permute-done | bytes 589856 | tf_op jit(solution)/shard_map/ppermute | solution.py:266
  45.2 1.1 collective-permute-start.19
  46.3 2.4 %collective-permute-start.21 = (bf16[2,9,32,128]{3,2,1,0:T(8,128)(2,1)S(1)}, bf16[2,9,32,128]{3,2,1,0:T(8,128)(2,1)S(1)}, u32[]{:S(2)}, u32[]{:S(2)}) collective-permute-start(bf16[2,9,32,128]{3,2,1,0:T(8,128)(2,1)S(1)} %get-tuple-element.137), channel_id=1, source_target_pairs={{0,12},{1,11},{2,14},{3,9},{4,8},{5,15},{6,10},{7,13},{8,4},{9,3},... | collective-permute-start | bytes 442376 | tf_op jit(solution)/shard_map/ppermute | solution.py:261
  48.7 2.5 %collective-permute-done.18.refs_0_ = bf16[2,9,32,128]{3,2,1,0:T(8,128)(2,1)S(1)} collective-permute-done((bf16[2,9,32,128]{3,2,1,0:T(8,128)(2,1)S(1)}, bf16[2,9,32,128]{3,2,1,0:T(8,128)(2,1)S(1)}, u32[]{:S(2)}, u32[]{:S(2)}) %collective-permute-start.18) | collective-permute-done | bytes 147488 | tf_op jit(solution)/shard_map/ppermute | solution.py:261
  51.2 0.7 collective-permute-done.19.refs_1_
  51.9 0.9 collective-permute-done.20.refs_2_
  52.7 2.2 %collective-permute-done.21.refs_3_ = bf16[2,9,32,128]{3,2,1,0:T(8,128)(2,1)S(1)} collective-permute-done((bf16[2,9,32,128]{3,2,1,0:T(8,128)(2,1)S(1)}, bf16[2,9,32,128]{3,2,1,0:T(8,128)(2,1)S(1)}, u32[]{:S(2)}, u32[]{:S(2)}) %collective-permute-start.21) | collective-permute-done | bytes 147488 | tf_op jit(solution)/shard_map/ppermute | solution.py:261
  55.3 0.9 collective-permute-start.24
  56.1 1.5 %collective-permute-start.25 = (bf16[2,9,32,128]{3,2,1,0:T(8,128)(2,1)S(1)}, bf16[2,9,32,128]{3,2,1,0:T(8,128)(2,1)S(1)}, u32[]{:S(2)}, u32[]{:S(2)}) collective-permute-start(bf16[2,9,32,128]{3,2,1,0:T(8,128)(2,1)S(1)} %get-tuple-element.153), channel_id=1, source_target_pairs={{0,8},{1,3},{2,10},{3,1},{4,12},{5,7},{6,14},{7,5},{8,0},{9,11},{1... | collective-permute-start | bytes 442376 | tf_op jit(solution)/shard_map/ppermute | solution.py:261
  58.1 0.7 collective-permute-done.26.inner_ref
  59.1 2.0 %collective-permute-done.23.refs_0_ = bf16[2,9,32,128]{3,2,1,0:T(8,128)(2,1)S(1)} collective-permute-done((bf16[2,9,32,128]{3,2,1,0:T(8,128)(2,1)S(1)}, bf16[2,9,32,128]{3,2,1,0:T(8,128)(2,1)S(1)}, u32[]{:S(2)}, u32[]{:S(2)}) %collective-permute-start.23) | collective-permute-done | bytes 147488 | tf_op jit(solution)/shard_map/ppermute | solution.py:261
  61.4 1.4 %collective-permute-start.28 = (bf16[9,32,128]{2,1,0:T(8,128)(2,1)S(1)}, bf16[9,32,128]{2,1,0:T(8,128)(2,1)S(1)}, u32[]{:S(2)}, u32[]{:S(2)}) collective-permute-start(bf16[9,32,128]{2,1,0:T(8,128)(2,1)S(1)} %get-tuple-element.162), channel_id=1, source_target_pairs={{0,16},{1,17},{2,18},{3,19},{4,20},{5,21},{6,22},{7,23},{8,24},{9,... | collective-permute-start | bytes 221192 | tf_op jit(solution)/shard_map/ppermute | solution.py:257
  62.7 4.0 %collective-permute-done.28.rest_0_ = bf16[9,32,128]{2,1,0:T(8,128)(2,1)S(1)} collective-permute-done((bf16[9,32,128]{2,1,0:T(8,128)(2,1)S(1)}, bf16[9,32,128]{2,1,0:T(8,128)(2,1)S(1)}, u32[]{:S(2)}, u32[]{:S(2)}) %collective-permute-start.28) | collective-permute-done | bytes 73760 | tf_op jit(solution)/shard_map/ppermute | solution.py:257
  66.7 1.6 %shard_map.105 = (bf16[8,32,256]{2,1,0:T(8,128)(2,1)}, bf16[9,32,128]{2,1,0:T(8,128)(2,1)S(1)}, bf16[1,32,256]{2,1,0:T(8,128)(2,1)S(1)}, bf16[1,32,256]{2,1,0:T(8,128)(2,1)S(1)}) custom-call(s32[12]{0:T(128)S(1)} %copy-done.8, f32[8,32,256]{2,1,0:T(8,128)S(1)} %shard_map.98.near_ref, f32[2,32,256]{2,1,0:T(8,128)S(1)} %shard_map.103.edge_ref, ...), custom_call_target="tpu_custom_call" | custom-call | tf_op jit(solution)/shard_map/pallas_call | solution.py:417
  68.3 1.4 %collective-permute-start.29 = (bf16[9,32,128]{2,1,0:T(8,128)(2,1)S(1)}, bf16[9,32,128]{2,1,0:T(8,128)(2,1)S(1)}, u32[]{:S(2)}, u32[]{:S(2)}) collective-permute-start(bf16[9,32,128]{2,1,0:T(8,128)(2,1)S(1)} %get-tuple-element.164.refs_0_), channel_id=1, source_target_pairs={{0,16},{1,17},{2,18},{3,19},{4,20},{5,21},{6,22},{7,23},{8,24},{9,... | collective-permute-start | bytes 221192 | tf_op jit(solution)/shard_map/ppermute | solution.py:257
  69.7 3.9 %collective-permute-done.29.refs_1_ = bf16[9,32,128]{2,1,0:T(8,128)(2,1)S(1)} collective-permute-done((bf16[9,32,128]{2,1,0:T(8,128)(2,1)S(1)}, bf16[9,32,128]{2,1,0:T(8,128)(2,1)S(1)}, u32[]{:S(2)}, u32[]{:S(2)}) %collective-permute-start.29) | collective-permute-done | bytes 73760 | tf_op jit(solution)/shard_map/ppermute | solution.py:257
  73.5 1.5 %collective-permute-start.32 = (bf16[2,9,32,128]{3,2,1,0:T(8,128)(2,1)S(1)}, bf16[2,9,32,128]{3,2,1,0:T(8,128)(2,1)S(1)}, u32[]{:S(2)}, u32[]{:S(2)}) collective-permute-start(bf16[2,9,32,128]{3,2,1,0:T(8,128)(2,1)S(1)} %shard_map.106.refs_0_), channel_id=1, source_target_pairs={{0,8},{1,3},{2,10},{3,1},{4,12},{5,7},{6,14},{7,5},{8,0},{9,11},{1... | collective-permute-start | bytes 442376 | tf_op jit(solution)/shard_map/ppermute | solution.py:261
  75.1 0.7 collective-permute-start.31
  75.8 1.8 %collective-permute-start.30 = (bf16[2,9,32,128]{3,2,1,0:T(8,128)(2,1)S(1)}, bf16[2,9,32,128]{3,2,1,0:T(8,128)(2,1)S(1)}, u32[]{:S(2)}, u32[]{:S(2)}) collective-permute-start(bf16[2,9,32,128]{3,2,1,0:T(8,128)(2,1)S(1)} %shard_map.106.refs_0_), channel_id=1, source_target_pairs={{0,2},{1,5},{2,0},{3,7},{4,6},{5,1},{6,4},{7,3},{8,10},{9,13},{10,... | collective-permute-start | bytes 442376 | tf_op jit(solution)/shard_map/ppermute | solution.py:261
  77.5 0.9 copy-done.6
  78.5 0.6 shard_map.107.near_ref
  79.0 1.6 %collective-permute-start.36 = (bf16[2,9,32,128]{3,2,1,0:T(8,128)(2,1)S(1)}, bf16[2,9,32,128]{3,2,1,0:T(8,128)(2,1)S(1)}, u32[]{:S(2)}, u32[]{:S(2)}) collective-permute-start(bf16[2,9,32,128]{3,2,1,0:T(8,128)(2,1)S(1)} %shard_map.106.refs_0_), channel_id=1, source_target_pairs={{0,14},{1,15},{2,12},{3,13},{4,10},{5,11},{6,8},{7,9},{8,6},{9,7},... | collective-permute-start | bytes 442376 | tf_op jit(solution)/shard_map/ppermute | solution.py:261
  80.6 0.6 collective-permute-done.31.refs_2_
  81.2 1.0 collective-permute-done.30.refs_1_
  82.2 1.2 collective-permute-start.33
  83.4 1.3 %collective-permute-start.37 = (bf16[1,32,256]{2,1,0:T(8,128)(2,1)S(1)}, bf16[1,32,256]{2,1,0:T(8,128)(2,1)S(1)}, u32[]{:S(2)}, u32[]{:S(2)}) collective-permute-start(bf16[1,32,256]{2,1,0:T(8,128)(2,1)S(1)} %get-tuple-element.170), channel_id=1, source_target_pairs={{1,3},{3,5},{5,7},{7,9},{9,11},{11,13},{13,15},{15,17},{17,19},{19... | collective-permute-start | bytes 49160 | tf_op jit(solution)/shard_map/ppermute | solution.py:394
  84.7 3.8 %collective-permute-start.35 = (bf16[2,9,32,128]{3,2,1,0:T(8,128)(2,1)S(1)}, bf16[2,9,32,128]{3,2,1,0:T(8,128)(2,1)S(1)}, u32[]{:S(2)}, u32[]{:S(2)}) collective-permute-start(bf16[2,9,32,128]{3,2,1,0:T(8,128)(2,1)S(1)} %collective-permute-done.31.refs_2_), channel_id=1, source_target_pairs={{0,8},{1,3},{2,10},{3,1},{4,12},{5,7},{6,14},{7,5},{8,0},{9,11},{1... | collective-permute-start | bytes 442376 | tf_op jit(solution)/shard_map/ppermute | solution.py:261
  88.5 0.5 collective-permute-done.37
  89.6 2.0 %collective-permute-done.35.refs_6_ = bf16[2,9,32,128]{3,2,1,0:T(8,128)(2,1)S(1)} collective-permute-done((bf16[2,9,32,128]{3,2,1,0:T(8,128)(2,1)S(1)}, bf16[2,9,32,128]{3,2,1,0:T(8,128)(2,1)S(1)}, u32[]{:S(2)}, u32[]{:S(2)}) %collective-permute-start.35) | collective-permute-done | bytes 147488 | tf_op jit(solution)/shard_map/ppermute | solution.py:261
  91.7 1.9 %collective-permute-done.34.refs_5_ = bf16[2,9,32,128]{3,2,1,0:T(8,128)(2,1)S(1)} collective-permute-done((bf16[2,9,32,128]{3,2,1,0:T(8,128)(2,1)S(1)}, bf16[2,9,32,128]{3,2,1,0:T(8,128)(2,1)S(1)}, u32[]{:S(2)}, u32[]{:S(2)}) %collective-permute-start.34) | collective-permute-done | bytes 147488 | tf_op jit(solution)/shard_map/ppermute | solution.py:261
  95.7 3.6 %shard_map.108 = (bf16[4,2,9,32,128]{4,3,2,1,0:T(8,128)(2,1)S(1)}, bf16[4,2,9,32,128]{4,3,2,1,0:T(8,128)(2,1)S(1)}, bf16[4,2,9,32,128]{4,3,2,1,0:T(8,128)(2,1)S(1)}, bf16[4,2,9,32,128]{4,3,2,1,0:T(8,128)(2,1)S(1)}) custom-call(s32[128]{0:T(128)S(1)} %bitcast.5, s32[128]{0:T(128)S(1)} %bitcast.7, bf16[128,96,96]{2,1,0:T(8,128)(2,1)S(1)} %copy-done.1, ...), custom_call_target="tpu_custom_call" | custom-call | flops 75497472 | bytes 10485760 | tf_op jit(solution)/shard_map/pallas_call | solution.py:397
  99.7 1.7 %collective-permute-done.46.swap_ref = bf16[4,2,9,32,128]{4,3,2,1,0:T(8,128)(2,1)S(1)} collective-permute-done((bf16[4,2,9,32,128]{4,3,2,1,0:T(8,128)(2,1)S(1)}, bf16[4,2,9,32,128]{4,3,2,1,0:T(8,128)(2,1)S(1)}, u32[]{:S(2)}, u32[]{:S(2)}) %collective-permute-start.46) | collective-permute-done | bytes 589856 | tf_op jit(solution)/shard_map/ppermute | solution.py:266
  101.9 0.9 collective-permute-start.47
  103.1 0.6 collective-permute-start.49
  103.8 1.6 %collective-permute-start.50 = (bf16[2,9,32,128]{3,2,1,0:T(8,128)(2,1)S(1)}, bf16[2,9,32,128]{3,2,1,0:T(8,128)(2,1)S(1)}, u32[]{:S(2)}, u32[]{:S(2)}) collective-permute-start(bf16[2,9,32,128]{3,2,1,0:T(8,128)(2,1)S(1)} %get-tuple-element.190), channel_id=1, source_target_pairs={{0,12},{1,11},{2,14},{3,9},{4,8},{5,15},{6,10},{7,13},{8,4},{9,3},... | collective-permute-start | bytes 442376 | tf_op jit(solution)/shard_map/ppermute | solution.py:261
  105.4 2.8 %collective-permute-done.47.refs_0_ = bf16[2,9,32,128]{3,2,1,0:T(8,128)(2,1)S(1)} collective-permute-done((bf16[2,9,32,128]{3,2,1,0:T(8,128)(2,1)S(1)}, bf16[2,9,32,128]{3,2,1,0:T(8,128)(2,1)S(1)}, u32[]{:S(2)}, u32[]{:S(2)}) %collective-permute-start.47) | collective-permute-done | bytes 147488 | tf_op jit(solution)/shard_map/ppermute | solution.py:261
  108.3 1.1 collective-permute-done.48.refs_1_
  109.8 1.9 %collective-permute-done.50.refs_3_ = bf16[2,9,32,128]{3,2,1,0:T(8,128)(2,1)S(1)} collective-permute-done((bf16[2,9,32,128]{3,2,1,0:T(8,128)(2,1)S(1)}, bf16[2,9,32,128]{3,2,1,0:T(8,128)(2,1)S(1)}, u32[]{:S(2)}, u32[]{:S(2)}) %collective-permute-start.50) | collective-permute-done | bytes 147488 | tf_op jit(solution)/shard_map/ppermute | solution.py:261
  111.9 0.5 collective-permute-start.52
  112.4 1.2 collective-permute-start.53
  113.6 0.7 collective-permute-start.54
  114.8 0.7 collective-permute-done.55.inner_ref
  115.8 1.3 %collective-permute-done.52.refs_0_ = bf16[2,9,32,128]{3,2,1,0:T(8,128)(2,1)S(1)} collective-permute-done((bf16[2,9,32,128]{3,2,1,0:T(8,128)(2,1)S(1)}, bf16[2,9,32,128]{3,2,1,0:T(8,128)(2,1)S(1)}, u32[]{:S(2)}, u32[]{:S(2)}) %collective-permute-start.52) | collective-permute-done | bytes 147488 | tf_op jit(solution)/shard_map/ppermute | solution.py:261
  117.5 1.2 collective-permute-done.54.refs_2_
  118.8 1.6 %collective-permute-start.57 = (bf16[9,32,128]{2,1,0:T(8,128)(2,1)S(1)}, bf16[9,32,128]{2,1,0:T(8,128)(2,1)S(1)}, u32[]{:S(2)}, u32[]{:S(2)}) collective-permute-start(bf16[9,32,128]{2,1,0:T(8,128)(2,1)S(1)} %get-tuple-element.215), channel_id=1, source_target_pairs={{0,16},{1,17},{2,18},{3,19},{4,20},{5,21},{6,22},{7,23},{8,24},{9,... | collective-permute-start | bytes 221192 | tf_op jit(solution)/shard_map/ppermute | solution.py:257
  120.4 4.5 %collective-permute-done.57.rest_0_ = bf16[9,32,128]{2,1,0:T(8,128)(2,1)S(1)} collective-permute-done((bf16[9,32,128]{2,1,0:T(8,128)(2,1)S(1)}, bf16[9,32,128]{2,1,0:T(8,128)(2,1)S(1)}, u32[]{:S(2)}, u32[]{:S(2)}) %collective-permute-start.57) | collective-permute-done | bytes 73760 | tf_op jit(solution)/shard_map/ppermute | solution.py:257
  124.9 1.6 %shard_map.113 = bf16[8,32,256]{2,1,0:T(8,128)(2,1)} custom-call(s32[12]{0:T(128)S(1)} %copy-done.8, f32[8,32,256]{2,1,0:T(8,128)S(1)} %shard_map.107.near_ref, f32[2,32,256]{2,1,0:T(8,128)S(1)} %shard_map.111.edge_ref, bf16[8,96,256]{2,1,0:T(8,128)(2,1)S(1)} %copy-done.2, bf16[8,96,96]{2,1,0:T(8,128)(2,1)S(1)} %copy-done.3, ...), custom_call_target="tpu_custom_call" | custom-call | tf_op jit(solution)/shard_map/pallas_call | solution.py:417
  (98 shorter events, 11.9 us)
Async XLA Ops:
  3.5 15.0 %copy-start = (bf16[8,3,256,256]{3,2,1,0:T(8,128)(2,1)S(1)}, bf16[8,3,256,256]{3,2,1,0:T(8,128)(2,1)}, u32[]{:S(2)}) copy-start(bf16[8,3,256,256]{3,2,1,0:T(8,128)(2,1)} %last_ref.3) | copy-start | bytes 9437188
  3.6 15.0 %copy-start.4 = (bf16[8,32,256]{2,1,0:T(8,128)(2,1)S(1)}, bf16[8,32,256]{2,1,0:T(8,128)(2,1)}, u32[]{:S(2)}) copy-start(bf16[8,32,256]{2,1,0:T(8,128)(2,1)} %v_ref.1) | copy-start | bytes 393220
  3.6 9.5 %collective-permute-start = (bf16[9,32,128]{2,1,0:T(8,128)(2,1)}, bf16[9,32,128]{2,1,0:T(8,128)(2,1)S(1)}, u32[]{:S(2)}, u32[]{:S(2)}) collective-permute-start(bf16[9,32,128]{2,1,0:T(8,128)(2,1)} %get-tuple-element.109.__.refs_0_), channel_id=1, source_target_pairs={{0,16},{1,17},{2,18},{3,19},{4,20},{5,21},{6,22},{7,23},{8,24},{9,... | collective-permute-start | bytes 221192 | tf_op jit(solution)/shard_map/ppermute | solution.py:257
  12.4 25.5 %copy-start.9 = (s32[128]{0:T(128)S(1)}, s32[128]{0:T(128)}, u32[]{:S(2)}) copy-start(s32[128]{0:T(128)} %param.14) | copy-start | bytes 1540
  12.4 25.5 %copy-start.10 = (s32[128]{0:T(128)S(1)}, s32[128]{0:T(128)}, u32[]{:S(2)}) copy-start(s32[128]{0:T(128)} %param.15) | copy-start | bytes 1540
  13.0 26.0 %copy-start.1 = (bf16[128,96,96]{2,1,0:T(8,128)(2,1)S(1)}, bf16[128,96,96]{2,1,0:T(8,128)(2,1)}, u32[]{:S(2)}) copy-start(bf16[128,96,96]{2,1,0:T(8,128)(2,1)} %copy.10._.coupling_ref) | copy-start | bytes 7077892
  13.9 6.6 %collective-permute-start.3 = (bf16[2,9,32,128]{3,2,1,0:T(8,128)(2,1)S(1)}, bf16[2,9,32,128]{3,2,1,0:T(8,128)(2,1)S(1)}, u32[]{:S(2)}, u32[]{:S(2)}) collective-permute-start(bf16[2,9,32,128]{3,2,1,0:T(8,128)(2,1)S(1)} %shard_map.97.refs_0_), channel_id=1, source_target_pairs={{0,8},{1,3},{2,10},{3,1},{4,12},{5,7},{6,14},{7,5},{8,0},{9,11},{1... | collective-permute-start | bytes 442376 | tf_op jit(solution)/shard_map/ppermute | solution.py:261
  15.5 6.9 %collective-permute-start.2 = (bf16[2,9,32,128]{3,2,1,0:T(8,128)(2,1)S(1)}, bf16[2,9,32,128]{3,2,1,0:T(8,128)(2,1)S(1)}, u32[]{:S(2)}, u32[]{:S(2)}) collective-permute-start(bf16[2,9,32,128]{3,2,1,0:T(8,128)(2,1)S(1)} %shard_map.97.refs_0_), channel_id=1, source_target_pairs={{0,4},{1,9},{2,6},{3,11},{4,0},{5,13},{6,2},{7,15},{8,12},{9,1},{1... | collective-permute-start | bytes 442376 | tf_op jit(solution)/shard_map/ppermute | solution.py:261
  17.0 7.3 %collective-permute-start.1 = (bf16[2,9,32,128]{3,2,1,0:T(8,128)(2,1)S(1)}, bf16[2,9,32,128]{3,2,1,0:T(8,128)(2,1)S(1)}, u32[]{:S(2)}, u32[]{:S(2)}) collective-permute-start(bf16[2,9,32,128]{3,2,1,0:T(8,128)(2,1)S(1)} %shard_map.97.refs_0_), channel_id=1, source_target_pairs={{0,2},{1,5},{2,0},{3,7},{4,6},{5,1},{6,4},{7,3},{8,10},{9,13},{10,... | collective-permute-start | bytes 442376 | tf_op jit(solution)/shard_map/ppermute | solution.py:261
  19.1 12.6 %collective-permute-start.7 = (bf16[2,9,32,128]{3,2,1,0:T(8,128)(2,1)S(1)}, bf16[2,9,32,128]{3,2,1,0:T(8,128)(2,1)S(1)}, u32[]{:S(2)}, u32[]{:S(2)}) collective-permute-start(bf16[2,9,32,128]{3,2,1,0:T(8,128)(2,1)S(1)} %shard_map.97.refs_0_), channel_id=1, source_target_pairs={{0,14},{1,15},{2,12},{3,13},{4,10},{5,11},{6,8},{7,9},{8,6},{9,7},... | collective-permute-start | bytes 442376 | tf_op jit(solution)/shard_map/ppermute | solution.py:261
  24.4 7.9 %collective-permute-start.4 = (bf16[2,9,32,128]{3,2,1,0:T(8,128)(2,1)S(1)}, bf16[2,9,32,128]{3,2,1,0:T(8,128)(2,1)S(1)}, u32[]{:S(2)}, u32[]{:S(2)}) collective-permute-start(bf16[2,9,32,128]{3,2,1,0:T(8,128)(2,1)S(1)} %collective-permute-done.1.refs_1_), channel_id=1, source_target_pairs={{0,4},{1,9},{2,6},{3,11},{4,0},{5,13},{6,2},{7,15},{8,12},{9,1},{1... | collective-permute-start | bytes 442376 | tf_op jit(solution)/shard_map/ppermute | solution.py:261
  24.9 6.9 %collective-permute-start.8 = (bf16[1,32,256]{2,1,0:T(8,128)(2,1)S(1)}, bf16[1,32,256]{2,1,0:T(8,128)(2,1)S(1)}, u32[]{:S(2)}, u32[]{:S(2)}) collective-permute-start(bf16[1,32,256]{2,1,0:T(8,128)(2,1)S(1)} %copy-done.12), channel_id=1, source_target_pairs={{1,3},{3,5},{5,7},{7,9},{9,11},{11,13},{13,15},{15,17},{17,19},{19... | collective-permute-start | bytes 49160 | tf_op jit(solution)/shard_map/ppermute | solution.py:394
  26.1 8.8 %collective-permute-start.6 = (bf16[2,9,32,128]{3,2,1,0:T(8,128)(2,1)S(1)}, bf16[2,9,32,128]{3,2,1,0:T(8,128)(2,1)S(1)}, u32[]{:S(2)}, u32[]{:S(2)}) collective-permute-start(bf16[2,9,32,128]{3,2,1,0:T(8,128)(2,1)S(1)} %collective-permute-done.2.refs_2_), channel_id=1, source_target_pairs={{0,8},{1,3},{2,10},{3,1},{4,12},{5,7},{6,14},{7,5},{8,0},{9,11},{1... | collective-permute-start | bytes 442376 | tf_op jit(solution)/shard_map/ppermute | solution.py:261
  31.7 5.1 %collective-permute-start.5 = (bf16[2,9,32,128]{3,2,1,0:T(8,128)(2,1)S(1)}, bf16[2,9,32,128]{3,2,1,0:T(8,128)(2,1)S(1)}, u32[]{:S(2)}, u32[]{:S(2)}) collective-permute-start(bf16[2,9,32,128]{3,2,1,0:T(8,128)(2,1)S(1)} %collective-permute-done.3.refs_4_), channel_id=1, source_target_pairs={{0,2},{1,5},{2,0},{3,7},{4,6},{5,1},{6,4},{7,3},{8,10},{9,13},{10,... | collective-permute-start | bytes 442376 | tf_op jit(solution)/shard_map/ppermute | solution.py:261
  31.7 5.1 %collective-permute-start.9 = (bf16[2,9,32,128]{3,2,1,0:T(8,128)(2,1)S(1)}, bf16[2,9,32,128]{3,2,1,0:T(8,128)(2,1)S(1)}, u32[]{:S(2)}, u32[]{:S(2)}) collective-permute-start(bf16[2,9,32,128]{3,2,1,0:T(8,128)(2,1)S(1)} %shard_map.97.refs_0_), channel_id=1, source_target_pairs={{0,1},{1,0},{2,3},{3,2},{4,5},{5,4},{6,7},{7,6},{8,9},{9,8},{10,11... | collective-permute-start | bytes 442376 | tf_op jit(solution)/shard_map/ppermute | solution.py:266
  31.8 5.6 %collective-permute-start.10 = (bf16[2,9,32,128]{3,2,1,0:T(8,128)(2,1)S(1)}, bf16[2,9,32,128]{3,2,1,0:T(8,128)(2,1)S(1)}, u32[]{:S(2)}, u32[]{:S(2)}) collective-permute-start(bf16[2,9,32,128]{3,2,1,0:T(8,128)(2,1)S(1)} %collective-permute-done.1.refs_1_), channel_id=1, source_target_pairs={{0,1},{1,0},{2,3},{3,2},{4,5},{5,4},{6,7},{7,6},{8,9},{9,8},{10,11... | collective-permute-start | bytes 442376 | tf_op jit(solution)/shard_map/ppermute | solution.py:266
  32.3 5.2 %collective-permute-start.11 = (bf16[2,9,32,128]{3,2,1,0:T(8,128)(2,1)S(1)}, bf16[2,9,32,128]{3,2,1,0:T(8,128)(2,1)S(1)}, u32[]{:S(2)}, u32[]{:S(2)}) collective-permute-start(bf16[2,9,32,128]{3,2,1,0:T(8,128)(2,1)S(1)} %collective-permute-done.2.refs_2_), channel_id=1, source_target_pairs={{0,1},{1,0},{2,3},{3,2},{4,5},{5,4},{6,7},{7,6},{8,9},{9,8},{10,11... | collective-permute-start | bytes 442376 | tf_op jit(solution)/shard_map/ppermute | solution.py:266
  34.9 3.0 %collective-permute-start.13 = (bf16[2,9,32,128]{3,2,1,0:T(8,128)(2,1)S(1)}, bf16[2,9,32,128]{3,2,1,0:T(8,128)(2,1)S(1)}, u32[]{:S(2)}, u32[]{:S(2)}) collective-permute-start(bf16[2,9,32,128]{3,2,1,0:T(8,128)(2,1)S(1)} %collective-permute-done.3.refs_4_), channel_id=1, source_target_pairs={{0,1},{1,0},{2,3},{3,2},{4,5},{5,4},{6,7},{7,6},{8,9},{9,8},{10,11... | collective-permute-start | bytes 442376 | tf_op jit(solution)/shard_map/ppermute | solution.py:266
  36.9 1.4 %collective-permute-start.12 = (bf16[2,9,32,128]{3,2,1,0:T(8,128)(2,1)S(1)}, bf16[2,9,32,128]{3,2,1,0:T(8,128)(2,1)S(1)}, u32[]{:S(2)}, u32[]{:S(2)}) collective-permute-start(bf16[2,9,32,128]{3,2,1,0:T(8,128)(2,1)S(1)} %collective-permute-done.4.refs_3_), channel_id=1, source_target_pairs={{0,1},{1,0},{2,3},{3,2},{4,5},{5,4},{6,7},{7,6},{8,9},{9,8},{10,11... | collective-permute-start | bytes 442376 | tf_op jit(solution)/shard_map/ppermute | solution.py:266
  36.9 1.6 %collective-permute-start.14 = (bf16[2,9,32,128]{3,2,1,0:T(8,128)(2,1)S(1)}, bf16[2,9,32,128]{3,2,1,0:T(8,128)(2,1)S(1)}, u32[]{:S(2)}, u32[]{:S(2)}) collective-permute-start(bf16[2,9,32,128]{3,2,1,0:T(8,128)(2,1)S(1)} %collective-permute-done.5.refs_5_), channel_id=1, source_target_pairs={{0,1},{1,0},{2,3},{3,2},{4,5},{5,4},{6,7},{7,6},{8,9},{9,8},{10,11... | collective-permute-start | bytes 442376 | tf_op jit(solution)/shard_map/ppermute | solution.py:266
  37.4 1.4 %collective-permute-start.15 = (bf16[2,9,32,128]{3,2,1,0:T(8,128)(2,1)S(1)}, bf16[2,9,32,128]{3,2,1,0:T(8,128)(2,1)S(1)}, u32[]{:S(2)}, u32[]{:S(2)}) collective-permute-start(bf16[2,9,32,128]{3,2,1,0:T(8,128)(2,1)S(1)} %collective-permute-done.6.refs_6_), channel_id=1, source_target_pairs={{0,1},{1,0},{2,3},{3,2},{4,5},{5,4},{6,7},{7,6},{8,9},{9,8},{10,11... | collective-permute-start | bytes 442376 | tf_op jit(solution)/shard_map/ppermute | solution.py:266
  37.5 1.5 %collective-permute-start.16 = (bf16[2,9,32,128]{3,2,1,0:T(8,128)(2,1)S(1)}, bf16[2,9,32,128]{3,2,1,0:T(8,128)(2,1)S(1)}, u32[]{:S(2)}, u32[]{:S(2)}) collective-permute-start(bf16[2,9,32,128]{3,2,1,0:T(8,128)(2,1)S(1)} %collective-permute-done.7.refs_7_), channel_id=1, source_target_pairs={{0,1},{1,0},{2,3},{3,2},{4,5},{5,4},{6,7},{7,6},{8,9},{9,8},{10,11... | collective-permute-start | bytes 442376 | tf_op jit(solution)/shard_map/ppermute | solution.py:266
  39.0 18.6 %copy-start.11 = (bf16[1,32,256]{2,1,0:T(8,128)(2,1)S(1)}, bf16[1,32,256]{2,1,0:T(8,128)(2,1)}, u32[]{:S(2)}) copy-start(bf16[1,32,256]{2,1,0:T(8,128)(2,1)} %get-tuple-element.154) | copy-start | bytes 49156
  42.6 2.1 %collective-permute-start.17 = (bf16[4,2,9,32,128]{4,3,2,1,0:T(8,128)(2,1)S(1)}, bf16[4,2,9,32,128]{4,3,2,1,0:T(8,128)(2,1)S(1)}, u32[]{:S(2)}, u32[]{:S(2)}) collective-permute-start(bf16[4,2,9,32,128]{4,3,2,1,0:T(8,128)(2,1)S(1)} %get-tuple-element.128), channel_id=1, source_target_pairs={{0,1},{1,0},{2,3},{3,2},{4,5},{5,4},{6,7},{7,6},{8,9},{9,8},{10,11... | collective-permute-start | bytes 1769480 | tf_op jit(solution)/shard_map/ppermute | solution.py:266
  44.8 10.1 %collective-permute-start.22 = (bf16[4,2,9,32,128]{4,3,2,1,0:T(8,128)(2,1)S(1)}, bf16[4,2,9,32,128]{4,3,2,1,0:T(8,128)(2,1)S(1)}, u32[]{:S(2)}, u32[]{:S(2)}) collective-permute-start(bf16[4,2,9,32,128]{4,3,2,1,0:T(8,128)(2,1)S(1)} %get-tuple-element.138), channel_id=1, source_target_pairs={{0,1},{1,0},{2,3},{3,2},{4,5},{5,4},{6,7},{7,6},{8,9},{9,8},{10,11... | collective-permute-start | bytes 1769480 | tf_op jit(solution)/shard_map/ppermute | solution.py:266
  45.2 6.0 %collective-permute-start.18 = (bf16[2,9,32,128]{3,2,1,0:T(8,128)(2,1)S(1)}, bf16[2,9,32,128]{3,2,1,0:T(8,128)(2,1)S(1)}, u32[]{:S(2)}, u32[]{:S(2)}) collective-permute-start(bf16[2,9,32,128]{3,2,1,0:T(8,128)(2,1)S(1)} %get-tuple-element.134), channel_id=1, source_target_pairs={{0,4},{1,9},{2,6},{3,11},{4,0},{5,13},{6,2},{7,15},{8,12},{9,1},{1... | collective-permute-start | bytes 442376 | tf_op jit(solution)/shard_map/ppermute | solution.py:261
  45.2 6.7 %collective-permute-start.19 = (bf16[2,9,32,128]{3,2,1,0:T(8,128)(2,1)S(1)}, bf16[2,9,32,128]{3,2,1,0:T(8,128)(2,1)S(1)}, u32[]{:S(2)}, u32[]{:S(2)}) collective-permute-start(bf16[2,9,32,128]{3,2,1,0:T(8,128)(2,1)S(1)} %get-tuple-element.135), channel_id=1, source_target_pairs={{0,8},{1,3},{2,10},{3,1},{4,12},{5,7},{6,14},{7,5},{8,0},{9,11},{1... | collective-permute-start | bytes 442376 | tf_op jit(solution)/shard_map/ppermute | solution.py:261
  46.2 6.5 %collective-permute-start.20 = (bf16[2,9,32,128]{3,2,1,0:T(8,128)(2,1)S(1)}, bf16[2,9,32,128]{3,2,1,0:T(8,128)(2,1)S(1)}, u32[]{:S(2)}, u32[]{:S(2)}) collective-permute-start(bf16[2,9,32,128]{3,2,1,0:T(8,128)(2,1)S(1)} %get-tuple-element.136), channel_id=1, source_target_pairs={{0,2},{1,5},{2,0},{3,7},{4,6},{5,1},{6,4},{7,3},{8,10},{9,13},{10,... | collective-permute-start | bytes 442376 | tf_op jit(solution)/shard_map/ppermute | solution.py:261
  46.3 8.6 %collective-permute-start.21 = (bf16[2,9,32,128]{3,2,1,0:T(8,128)(2,1)S(1)}, bf16[2,9,32,128]{3,2,1,0:T(8,128)(2,1)S(1)}, u32[]{:S(2)}, u32[]{:S(2)}) collective-permute-start(bf16[2,9,32,128]{3,2,1,0:T(8,128)(2,1)S(1)} %get-tuple-element.137), channel_id=1, source_target_pairs={{0,12},{1,11},{2,14},{3,9},{4,8},{5,15},{6,10},{7,13},{8,4},{9,3},... | collective-permute-start | bytes 442376 | tf_op jit(solution)/shard_map/ppermute | solution.py:261
  55.2 5.9 %collective-permute-start.23 = (bf16[2,9,32,128]{3,2,1,0:T(8,128)(2,1)S(1)}, bf16[2,9,32,128]{3,2,1,0:T(8,128)(2,1)S(1)}, u32[]{:S(2)}, u32[]{:S(2)}) collective-permute-start(bf16[2,9,32,128]{3,2,1,0:T(8,128)(2,1)S(1)} %get-tuple-element.151), channel_id=1, source_target_pairs={{0,2},{1,5},{2,0},{3,7},{4,6},{5,1},{6,4},{7,3},{8,10},{9,13},{10,... | collective-permute-start | bytes 442376 | tf_op jit(solution)/shard_map/ppermute | solution.py:261
  55.3 5.8 %collective-permute-start.24 = (bf16[2,9,32,128]{3,2,1,0:T(8,128)(2,1)S(1)}, bf16[2,9,32,128]{3,2,1,0:T(8,128)(2,1)S(1)}, u32[]{:S(2)}, u32[]{:S(2)}) collective-permute-start(bf16[2,9,32,128]{3,2,1,0:T(8,128)(2,1)S(1)} %get-tuple-element.152), channel_id=1, source_target_pairs={{0,4},{1,9},{2,6},{3,11},{4,0},{5,13},{6,2},{7,15},{8,12},{9,1},{1... | collective-permute-start | bytes 442376 | tf_op jit(solution)/shard_map/ppermute | solution.py:261
  56.1 5.1 %collective-permute-start.25 = (bf16[2,9,32,128]{3,2,1,0:T(8,128)(2,1)S(1)}, bf16[2,9,32,128]{3,2,1,0:T(8,128)(2,1)S(1)}, u32[]{:S(2)}, u32[]{:S(2)}) collective-permute-start(bf16[2,9,32,128]{3,2,1,0:T(8,128)(2,1)S(1)} %get-tuple-element.153), channel_id=1, source_target_pairs={{0,8},{1,3},{2,10},{3,1},{4,12},{5,7},{6,14},{7,5},{8,0},{9,11},{1... | collective-permute-start | bytes 442376 | tf_op jit(solution)/shard_map/ppermute | solution.py:261
  57.6 1.2 collective-permute-start.26
  57.6 1.3 %collective-permute-start.27 = (bf16[1,32,256]{2,1,0:T(8,128)(2,1)S(1)}, bf16[1,32,256]{2,1,0:T(8,128)(2,1)S(1)}, u32[]{:S(2)}, u32[]{:S(2)}) collective-permute-start(bf16[1,32,256]{2,1,0:T(8,128)(2,1)S(1)} %collective-permute-done.8), channel_id=1, source_target_pairs={{0,1},{1,0},{2,3},{3,2},{4,5},{5,4},{6,7},{7,6},{8,9},{9,8},{10,11... | collective-permute-start | bytes 49160 | tf_op jit(solution)/shard_map/ppermute | solution.py:266
  61.4 5.3 %collective-permute-start.28 = (bf16[9,32,128]{2,1,0:T(8,128)(2,1)S(1)}, bf16[9,32,128]{2,1,0:T(8,128)(2,1)S(1)}, u32[]{:S(2)}, u32[]{:S(2)}) collective-permute-start(bf16[9,32,128]{2,1,0:T(8,128)(2,1)S(1)} %get-tuple-element.162), channel_id=1, source_target_pairs={{0,16},{1,17},{2,18},{3,19},{4,20},{5,21},{6,22},{7,23},{8,24},{9,... | collective-permute-start | bytes 221192 | tf_op jit(solution)/shard_map/ppermute | solution.py:257
  68.3 5.3 %collective-permute-start.29 = (bf16[9,32,128]{2,1,0:T(8,128)(2,1)S(1)}, bf16[9,32,128]{2,1,0:T(8,128)(2,1)S(1)}, u32[]{:S(2)}, u32[]{:S(2)}) collective-permute-start(bf16[9,32,128]{2,1,0:T(8,128)(2,1)S(1)} %get-tuple-element.164.refs_0_), channel_id=1, source_target_pairs={{0,16},{1,17},{2,18},{3,19},{4,20},{5,21},{6,22},{7,23},{8,24},{9,... | collective-permute-start | bytes 221192 | tf_op jit(solution)/shard_map/ppermute | solution.py:257
  73.5 7.1 %collective-permute-start.32 = (bf16[2,9,32,128]{3,2,1,0:T(8,128)(2,1)S(1)}, bf16[2,9,32,128]{3,2,1,0:T(8,128)(2,1)S(1)}, u32[]{:S(2)}, u32[]{:S(2)}) collective-permute-start(bf16[2,9,32,128]{3,2,1,0:T(8,128)(2,1)S(1)} %shard_map.106.refs_0_), channel_id=1, source_target_pairs={{0,8},{1,3},{2,10},{3,1},{4,12},{5,7},{6,14},{7,5},{8,0},{9,11},{1... | collective-permute-start | bytes 442376 | tf_op jit(solution)/shard_map/ppermute | solution.py:261
  75.1 6.1 %collective-permute-start.31 = (bf16[2,9,32,128]{3,2,1,0:T(8,128)(2,1)S(1)}, bf16[2,9,32,128]{3,2,1,0:T(8,128)(2,1)S(1)}, u32[]{:S(2)}, u32[]{:S(2)}) collective-permute-start(bf16[2,9,32,128]{3,2,1,0:T(8,128)(2,1)S(1)} %shard_map.106.refs_0_), channel_id=1, source_target_pairs={{0,4},{1,9},{2,6},{3,11},{4,0},{5,13},{6,2},{7,15},{8,12},{9,1},{1... | collective-permute-start | bytes 442376 | tf_op jit(solution)/shard_map/ppermute | solution.py:261
  75.8 6.4 %collective-permute-start.30 = (bf16[2,9,32,128]{3,2,1,0:T(8,128)(2,1)S(1)}, bf16[2,9,32,128]{3,2,1,0:T(8,128)(2,1)S(1)}, u32[]{:S(2)}, u32[]{:S(2)}) collective-permute-start(bf16[2,9,32,128]{3,2,1,0:T(8,128)(2,1)S(1)} %shard_map.106.refs_0_), channel_id=1, source_target_pairs={{0,2},{1,5},{2,0},{3,7},{4,6},{5,1},{6,4},{7,3},{8,10},{9,13},{10,... | collective-permute-start | bytes 442376 | tf_op jit(solution)/shard_map/ppermute | solution.py:261
  79.0 10.0 %collective-permute-start.36 = (bf16[2,9,32,128]{3,2,1,0:T(8,128)(2,1)S(1)}, bf16[2,9,32,128]{3,2,1,0:T(8,128)(2,1)S(1)}, u32[]{:S(2)}, u32[]{:S(2)}) collective-permute-start(bf16[2,9,32,128]{3,2,1,0:T(8,128)(2,1)S(1)} %shard_map.106.refs_0_), channel_id=1, source_target_pairs={{0,14},{1,15},{2,12},{3,13},{4,10},{5,11},{6,8},{7,9},{8,6},{9,7},... | collective-permute-start | bytes 442376 | tf_op jit(solution)/shard_map/ppermute | solution.py:261
  82.2 7.4 %collective-permute-start.33 = (bf16[2,9,32,128]{3,2,1,0:T(8,128)(2,1)S(1)}, bf16[2,9,32,128]{3,2,1,0:T(8,128)(2,1)S(1)}, u32[]{:S(2)}, u32[]{:S(2)}) collective-permute-start(bf16[2,9,32,128]{3,2,1,0:T(8,128)(2,1)S(1)} %collective-permute-done.30.refs_1_), channel_id=1, source_target_pairs={{0,4},{1,9},{2,6},{3,11},{4,0},{5,13},{6,2},{7,15},{8,12},{9,1},{1... | collective-permute-start | bytes 442376 | tf_op jit(solution)/shard_map/ppermute | solution.py:261
  83.4 5.6 %collective-permute-start.37 = (bf16[1,32,256]{2,1,0:T(8,128)(2,1)S(1)}, bf16[1,32,256]{2,1,0:T(8,128)(2,1)S(1)}, u32[]{:S(2)}, u32[]{:S(2)}) collective-permute-start(bf16[1,32,256]{2,1,0:T(8,128)(2,1)S(1)} %get-tuple-element.170), channel_id=1, source_target_pairs={{1,3},{3,5},{5,7},{7,9},{9,11},{11,13},{13,15},{15,17},{17,19},{19... | collective-permute-start | bytes 49160 | tf_op jit(solution)/shard_map/ppermute | solution.py:394
  84.7 7.0 %collective-permute-start.35 = (bf16[2,9,32,128]{3,2,1,0:T(8,128)(2,1)S(1)}, bf16[2,9,32,128]{3,2,1,0:T(8,128)(2,1)S(1)}, u32[]{:S(2)}, u32[]{:S(2)}) collective-permute-start(bf16[2,9,32,128]{3,2,1,0:T(8,128)(2,1)S(1)} %collective-permute-done.31.refs_2_), channel_id=1, source_target_pairs={{0,8},{1,3},{2,10},{3,1},{4,12},{5,7},{6,14},{7,5},{8,0},{9,11},{1... | collective-permute-start | bytes 442376 | tf_op jit(solution)/shard_map/ppermute | solution.py:261
  88.4 5.1 %collective-permute-start.34 = (bf16[2,9,32,128]{3,2,1,0:T(8,128)(2,1)S(1)}, bf16[2,9,32,128]{3,2,1,0:T(8,128)(2,1)S(1)}, u32[]{:S(2)}, u32[]{:S(2)}) collective-permute-start(bf16[2,9,32,128]{3,2,1,0:T(8,128)(2,1)S(1)} %collective-permute-done.32.refs_4_), channel_id=1, source_target_pairs={{0,2},{1,5},{2,0},{3,7},{4,6},{5,1},{6,4},{7,3},{8,10},{9,13},{10,... | collective-permute-start | bytes 442376 | tf_op jit(solution)/shard_map/ppermute | solution.py:261
  89.0 4.6 %collective-permute-start.38 = (bf16[2,9,32,128]{3,2,1,0:T(8,128)(2,1)S(1)}, bf16[2,9,32,128]{3,2,1,0:T(8,128)(2,1)S(1)}, u32[]{:S(2)}, u32[]{:S(2)}) collective-permute-start(bf16[2,9,32,128]{3,2,1,0:T(8,128)(2,1)S(1)} %shard_map.106.refs_0_), channel_id=1, source_target_pairs={{0,1},{1,0},{2,3},{3,2},{4,5},{5,4},{6,7},{7,6},{8,9},{9,8},{10,11... | collective-permute-start | bytes 442376 | tf_op jit(solution)/shard_map/ppermute | solution.py:266
  89.0 5.1 %collective-permute-start.39 = (bf16[2,9,32,128]{3,2,1,0:T(8,128)(2,1)S(1)}, bf16[2,9,32,128]{3,2,1,0:T(8,128)(2,1)S(1)}, u32[]{:S(2)}, u32[]{:S(2)}) collective-permute-start(bf16[2,9,32,128]{3,2,1,0:T(8,128)(2,1)S(1)} %collective-permute-done.30.refs_1_), channel_id=1, source_target_pairs={{0,1},{1,0},{2,3},{3,2},{4,5},{5,4},{6,7},{7,6},{8,9},{9,8},{10,11... | collective-permute-start | bytes 442376 | tf_op jit(solution)/shard_map/ppermute | solution.py:266
  89.5 4.6 %collective-permute-start.40 = (bf16[2,9,32,128]{3,2,1,0:T(8,128)(2,1)S(1)}, bf16[2,9,32,128]{3,2,1,0:T(8,128)(2,1)S(1)}, u32[]{:S(2)}, u32[]{:S(2)}) collective-permute-start(bf16[2,9,32,128]{3,2,1,0:T(8,128)(2,1)S(1)} %collective-permute-done.31.refs_2_), channel_id=1, source_target_pairs={{0,1},{1,0},{2,3},{3,2},{4,5},{5,4},{6,7},{7,6},{8,9},{9,8},{10,11... | collective-permute-start | bytes 442376 | tf_op jit(solution)/shard_map/ppermute | solution.py:266
  91.7 3.0 %collective-permute-start.42 = (bf16[2,9,32,128]{3,2,1,0:T(8,128)(2,1)S(1)}, bf16[2,9,32,128]{3,2,1,0:T(8,128)(2,1)S(1)}, u32[]{:S(2)}, u32[]{:S(2)}) collective-permute-start(bf16[2,9,32,128]{3,2,1,0:T(8,128)(2,1)S(1)} %collective-permute-done.32.refs_4_), channel_id=1, source_target_pairs={{0,1},{1,0},{2,3},{3,2},{4,5},{5,4},{6,7},{7,6},{8,9},{9,8},{10,11... | collective-permute-start | bytes 442376 | tf_op jit(solution)/shard_map/ppermute | solution.py:266
  93.6 1.4 %collective-permute-start.41 = (bf16[2,9,32,128]{3,2,1,0:T(8,128)(2,1)S(1)}, bf16[2,9,32,128]{3,2,1,0:T(8,128)(2,1)S(1)}, u32[]{:S(2)}, u32[]{:S(2)}) collective-permute-start(bf16[2,9,32,128]{3,2,1,0:T(8,128)(2,1)S(1)} %collective-permute-done.33.refs_3_), channel_id=1, source_target_pairs={{0,1},{1,0},{2,3},{3,2},{4,5},{5,4},{6,7},{7,6},{8,9},{9,8},{10,11... | collective-permute-start | bytes 442376 | tf_op jit(solution)/shard_map/ppermute | solution.py:266
  93.6 1.6 %collective-permute-start.43 = (bf16[2,9,32,128]{3,2,1,0:T(8,128)(2,1)S(1)}, bf16[2,9,32,128]{3,2,1,0:T(8,128)(2,1)S(1)}, u32[]{:S(2)}, u32[]{:S(2)}) collective-permute-start(bf16[2,9,32,128]{3,2,1,0:T(8,128)(2,1)S(1)} %collective-permute-done.34.refs_5_), channel_id=1, source_target_pairs={{0,1},{1,0},{2,3},{3,2},{4,5},{5,4},{6,7},{7,6},{8,9},{9,8},{10,11... | collective-permute-start | bytes 442376 | tf_op jit(solution)/shard_map/ppermute | solution.py:266
  94.1 1.4 %collective-permute-start.44 = (bf16[2,9,32,128]{3,2,1,0:T(8,128)(2,1)S(1)}, bf16[2,9,32,128]{3,2,1,0:T(8,128)(2,1)S(1)}, u32[]{:S(2)}, u32[]{:S(2)}) collective-permute-start(bf16[2,9,32,128]{3,2,1,0:T(8,128)(2,1)S(1)} %collective-permute-done.35.refs_6_), channel_id=1, source_target_pairs={{0,1},{1,0},{2,3},{3,2},{4,5},{5,4},{6,7},{7,6},{8,9},{9,8},{10,11... | collective-permute-start | bytes 442376 | tf_op jit(solution)/shard_map/ppermute | solution.py:266
  94.2 1.5 %collective-permute-start.45 = (bf16[2,9,32,128]{3,2,1,0:T(8,128)(2,1)S(1)}, bf16[2,9,32,128]{3,2,1,0:T(8,128)(2,1)S(1)}, u32[]{:S(2)}, u32[]{:S(2)}) collective-permute-start(bf16[2,9,32,128]{3,2,1,0:T(8,128)(2,1)S(1)} %collective-permute-done.36.refs_7_), channel_id=1, source_target_pairs={{0,1},{1,0},{2,3},{3,2},{4,5},{5,4},{6,7},{7,6},{8,9},{9,8},{10,11... | collective-permute-start | bytes 442376 | tf_op jit(solution)/shard_map/ppermute | solution.py:266
  99.3 2.1 %collective-permute-start.46 = (bf16[4,2,9,32,128]{4,3,2,1,0:T(8,128)(2,1)S(1)}, bf16[4,2,9,32,128]{4,3,2,1,0:T(8,128)(2,1)S(1)}, u32[]{:S(2)}, u32[]{:S(2)}) collective-permute-start(bf16[4,2,9,32,128]{4,3,2,1,0:T(8,128)(2,1)S(1)} %get-tuple-element.181), channel_id=1, source_target_pairs={{0,1},{1,0},{2,3},{3,2},{4,5},{5,4},{6,7},{7,6},{8,9},{9,8},{10,11... | collective-permute-start | bytes 1769480 | tf_op jit(solution)/shard_map/ppermute | solution.py:266
  101.5 10.1 %collective-permute-start.51 = (bf16[4,2,9,32,128]{4,3,2,1,0:T(8,128)(2,1)S(1)}, bf16[4,2,9,32,128]{4,3,2,1,0:T(8,128)(2,1)S(1)}, u32[]{:S(2)}, u32[]{:S(2)}) collective-permute-start(bf16[4,2,9,32,128]{4,3,2,1,0:T(8,128)(2,1)S(1)} %get-tuple-element.191), channel_id=1, source_target_pairs={{0,1},{1,0},{2,3},{3,2},{4,5},{5,4},{6,7},{7,6},{8,9},{9,8},{10,11... | collective-permute-start | bytes 1769480 | tf_op jit(solution)/shard_map/ppermute | solution.py:266
  101.9 6.4 %collective-permute-start.47 = (bf16[2,9,32,128]{3,2,1,0:T(8,128)(2,1)S(1)}, bf16[2,9,32,128]{3,2,1,0:T(8,128)(2,1)S(1)}, u32[]{:S(2)}, u32[]{:S(2)}) collective-permute-start(bf16[2,9,32,128]{3,2,1,0:T(8,128)(2,1)S(1)} %get-tuple-element.187), channel_id=1, source_target_pairs={{0,4},{1,9},{2,6},{3,11},{4,0},{5,13},{6,2},{7,15},{8,12},{9,1},{1... | collective-permute-start | bytes 442376 | tf_op jit(solution)/shard_map/ppermute | solution.py:261
  102.8 6.6 %collective-permute-start.48 = (bf16[2,9,32,128]{3,2,1,0:T(8,128)(2,1)S(1)}, bf16[2,9,32,128]{3,2,1,0:T(8,128)(2,1)S(1)}, u32[]{:S(2)}, u32[]{:S(2)}) collective-permute-start(bf16[2,9,32,128]{3,2,1,0:T(8,128)(2,1)S(1)} %get-tuple-element.188), channel_id=1, source_target_pairs={{0,8},{1,3},{2,10},{3,1},{4,12},{5,7},{6,14},{7,5},{8,0},{9,11},{1... | collective-permute-start | bytes 442376 | tf_op jit(solution)/shard_map/ppermute | solution.py:261
  103.1 6.7 %collective-permute-start.49 = (bf16[2,9,32,128]{3,2,1,0:T(8,128)(2,1)S(1)}, bf16[2,9,32,128]{3,2,1,0:T(8,128)(2,1)S(1)}, u32[]{:S(2)}, u32[]{:S(2)}) collective-permute-start(bf16[2,9,32,128]{3,2,1,0:T(8,128)(2,1)S(1)} %get-tuple-element.189), channel_id=1, source_target_pairs={{0,2},{1,5},{2,0},{3,7},{4,6},{5,1},{6,4},{7,3},{8,10},{9,13},{10,... | collective-permute-start | bytes 442376 | tf_op jit(solution)/shard_map/ppermute | solution.py:261
  103.8 7.9 %collective-permute-start.50 = (bf16[2,9,32,128]{3,2,1,0:T(8,128)(2,1)S(1)}, bf16[2,9,32,128]{3,2,1,0:T(8,128)(2,1)S(1)}, u32[]{:S(2)}, u32[]{:S(2)}) collective-permute-start(bf16[2,9,32,128]{3,2,1,0:T(8,128)(2,1)S(1)} %get-tuple-element.190), channel_id=1, source_target_pairs={{0,12},{1,11},{2,14},{3,9},{4,8},{5,15},{6,10},{7,13},{8,4},{9,3},... | collective-permute-start | bytes 442376 | tf_op jit(solution)/shard_map/ppermute | solution.py:261
  111.9 5.2 %collective-permute-start.52 = (bf16[2,9,32,128]{3,2,1,0:T(8,128)(2,1)S(1)}, bf16[2,9,32,128]{3,2,1,0:T(8,128)(2,1)S(1)}, u32[]{:S(2)}, u32[]{:S(2)}) collective-permute-start(bf16[2,9,32,128]{3,2,1,0:T(8,128)(2,1)S(1)} %get-tuple-element.204), channel_id=1, source_target_pairs={{0,2},{1,5},{2,0},{3,7},{4,6},{5,1},{6,4},{7,3},{8,10},{9,13},{10,... | collective-permute-start | bytes 442376 | tf_op jit(solution)/shard_map/ppermute | solution.py:261
  112.4 5.1 %collective-permute-start.53 = (bf16[2,9,32,128]{3,2,1,0:T(8,128)(2,1)S(1)}, bf16[2,9,32,128]{3,2,1,0:T(8,128)(2,1)S(1)}, u32[]{:S(2)}, u32[]{:S(2)}) collective-permute-start(bf16[2,9,32,128]{3,2,1,0:T(8,128)(2,1)S(1)} %get-tuple-element.205), channel_id=1, source_target_pairs={{0,4},{1,9},{2,6},{3,11},{4,0},{5,13},{6,2},{7,15},{8,12},{9,1},{1... | collective-permute-start | bytes 442376 | tf_op jit(solution)/shard_map/ppermute | solution.py:261
  113.6 5.1 %collective-permute-start.54 = (bf16[2,9,32,128]{3,2,1,0:T(8,128)(2,1)S(1)}, bf16[2,9,32,128]{3,2,1,0:T(8,128)(2,1)S(1)}, u32[]{:S(2)}, u32[]{:S(2)}) collective-permute-start(bf16[2,9,32,128]{3,2,1,0:T(8,128)(2,1)S(1)} %get-tuple-element.206), channel_id=1, source_target_pairs={{0,8},{1,3},{2,10},{3,1},{4,12},{5,7},{6,14},{7,5},{8,0},{9,11},{1... | collective-permute-start | bytes 442376 | tf_op jit(solution)/shard_map/ppermute | solution.py:261
  114.3 1.2 collective-permute-start.55
  114.3 1.3 %collective-permute-start.56 = (bf16[1,32,256]{2,1,0:T(8,128)(2,1)S(1)}, bf16[1,32,256]{2,1,0:T(8,128)(2,1)S(1)}, u32[]{:S(2)}, u32[]{:S(2)}) collective-permute-start(bf16[1,32,256]{2,1,0:T(8,128)(2,1)S(1)} %collective-permute-done.37), channel_id=1, source_target_pairs={{0,1},{1,0},{2,3},{3,2},{4,5},{5,4},{6,7},{7,6},{8,9},{9,8},{10,11... | collective-permute-start | bytes 49160 | tf_op jit(solution)/shard_map/ppermute | solution.py:266
  118.8 6.1 %collective-permute-start.57 = (bf16[9,32,128]{2,1,0:T(8,128)(2,1)S(1)}, bf16[9,32,128]{2,1,0:T(8,128)(2,1)S(1)}, u32[]{:S(2)}, u32[]{:S(2)}) collective-permute-start(bf16[9,32,128]{2,1,0:T(8,128)(2,1)S(1)} %get-tuple-element.215), channel_id=1, source_target_pairs={{0,16},{1,17},{2,18},{3,19},{4,20},{5,21},{6,22},{7,23},{8,24},{9,... | collective-permute-start | bytes 221192 | tf_op jit(solution)/shard_map/ppermute | solution.py:257
  (7 other events, 58.2 us)

commit v20 on v19

--- a/solution.py
+++ b/solution.py
@@ -384,14 +384,20 @@
 
     def apply_matrix(field_in, coeffs, inner, outer, coupling, with_coeffs):
         away = [swap_far(coeffs, s) for s in range(1, far)]
-        (column,) = first_join(relaid(coupling, coeffs), coeffs, *away) if with_coeffs else join(coeffs, *away)
+        if with_coeffs:
+            outer, away = barrier((lax.ppermute(outer, "clu", halo_pairs), away))
+            (column,) = first_join(relaid(coupling, coeffs), coeffs, *away)
+        else:
+            (column,) = join(coeffs, *away)
         got = {0: column, x: swap(column, x), y: swap(column, y), z: swap(column, z)}
         near_sum = near(field_in, near_field)
         got, near_sum = barrier((got, near_sum))
         corner = swap(column, x | y | z)
         other = {chip: swap_cores(part) for chip, part in got.items()}
         got |= {x | y: swap(got[x], y), y | z: swap(got[y], z), z | x: swap(got[z], x)}
-        got, corner, outer = barrier((got, corner, lax.ppermute(outer, "clu", halo_pairs)))
+        if not with_coeffs:
+            outer = lax.ppermute(outer, "clu", halo_pairs)
+        got, corner, outer = barrier((got, corner, outer))
         got[x | y | z] = corner
         other |= {chip: swap_cores(got[chip]) for chip in order[0]}
         totals = couple(

time: 127 us -> 127 us (level)
  waiting for transfers between devices: 52.6 us -> 56.7 us
  starting transfers between devices: 50.3 us -> 46.5 us
    ppermute x4, waiting for transfers between devices: 12.4 us -> 16.1 us  [swap_far(): lax.ppermute(part, 'clu', [(d, (d + shift * cube) % devices) for d in ran...]
    ppermute x4, starting transfers between devices: 8.42 us -> 5.66 us  [swap_far(): lax.ppermute(part, 'clu', [(d, (d + shift * cube) % devices) for d in ran...]
    unnamed x27 -> x25, local copies, waits for them, and re-layouts: 6.54 us -> 6.56 us
where the time goes in v20:
time: 127 us
  waiting for transfers between devices  56.7 us (45%)
  starting transfers between devices  46.5 us (37%)
  Pallas kernels  16.2 us (13%)
  local copies, waits for them, and re-layouts  6.56 us (5%)
    ppermute x28, waiting for transfers between devices, swap(): lax.ppermute(part, 'clu', [(d, d ^ (turned if d % cores else direction) *...  33.1 us
    ppermute x28, starting transfers between devices, swap(): lax.ppermute(part, 'clu', [(d, d ^ (turned if d % cores else direction) *...  32.5 us
    ppermute x4, waiting for transfers between devices, swap_far(): lax.ppermute(part, 'clu', [(d, (d + shift * cube) % devices) for d in ran...  16.1 us
    ppermute x24, waiting for transfers between devices, swap_cores(): return lax.ppermute(part, 'clu', [(d, d ^ 1) for d in range(devices)])  7.53 us
    pallas_call x2, Pallas kernels, apply_matrix(): couple(source_rows, target_rows, coupling, *[got[chip] for chip in range(...  7.2 us
    unnamed x25, local copies, waits for them, and re-layouts  6.56 us
    ppermute x4, starting transfers between devices, swap_far(): lax.ppermute(part, 'clu', [(d, (d + shift * cube) % devices) for d in ran...  5.66 us
    ppermute x24, starting transfers between devices, swap_cores(): return lax.ppermute(part, 'clu', [(d, d ^ 1) for d in range(devices)])  5.52 us
  transfers between devices with their start and end apart: 58, of which 40 were waited for; matrix products, arithmetic and copies ran while one was open for 4% of the time, Pallas kernels for 2%

profile of v20, /device:TPU:0, one launch (start us, length us, event | category | flops | bytes accessed | tf_op | source)
XLA Modules:
  0.0 126.8 jit_solution(224278304729138686)
XLA Ops:
  0.6 2.9 %shard_map.95 = (bf16[9,32,128]{2,1,0:T(8,128)(2,1)}, bf16[1,32,256]{2,1,0:T(8,128)(2,1)}, bf16[1,32,256]{2,1,0:T(8,128)(2,1)}) custom-call(s32[12]{0:T(128)} %ranks_ref.5, bf16[8,32,256]{2,1,0:T(8,128)(2,1)} %v_ref.1, bf16[8,96,256]{2,1,0:T(8,128)(2,1)} %basis_ref.3, bf16[8,96,96]{2,1,0:T(8,128)(2,1)} %transfer_ref.3), custom_call_target="tpu_custom_call" | custom-call | tf_op jit(solution)/shard_map/pallas_call | solution.py:289
  3.5 4.1 %collective-permute-start.1 = (bf16[9,32,128]{2,1,0:T(8,128)(2,1)}, bf16[9,32,128]{2,1,0:T(8,128)(2,1)S(1)}, u32[]{:S(2)}, u32[]{:S(2)}) collective-permute-start(bf16[9,32,128]{2,1,0:T(8,128)(2,1)} %get-tuple-element.111.__.refs_0_), channel_id=1, source_target_pairs={{0,16},{1,17},{2,18},{3,19},{4,20},{5,21},{6,22},{7,23},{8,24},{9,... | collective-permute-start | bytes 221192 | tf_op jit(solution)/shard_map/ppermute | solution.py:257
  7.6 1.5 %collective-permute-start = (bf16[1,32,256]{2,1,0:T(8,128)(2,1)}, bf16[1,32,256]{2,1,0:T(8,128)(2,1)S(1)}, u32[]{:S(2)}, u32[]{:S(2)}) collective-permute-start(bf16[1,32,256]{2,1,0:T(8,128)(2,1)} %get-tuple-element.112), channel_id=1, source_target_pairs={{1,3},{3,5},{5,7},{7,9},{9,11},{11,13},{13,15},{15,17},{17,19},{19... | collective-permute-start | bytes 49160 | tf_op jit(solution)/shard_map/ppermute | solution.py:388
  9.2 4.8 %copy.10._.coupling_ref = bf16[128,96,96]{2,1,0:T(8,128)(2,1)} copy(bf16[128,96,96]{0,2,1:T(8,128)(2,1)} %param.12) | data formatting | bytes 4718592 | tf_op args[4]
  14.0 0.6 shard_map.96._
  14.6 0.8 copy-done.7
  15.4 4.6 %collective-permute-start.4 = (bf16[2,9,32,128]{3,2,1,0:T(8,128)(2,1)S(1)}, bf16[2,9,32,128]{3,2,1,0:T(8,128)(2,1)S(1)}, u32[]{:S(2)}, u32[]{:S(2)}) collective-permute-start(bf16[2,9,32,128]{3,2,1,0:T(8,128)(2,1)S(1)} %shard_map.97.refs_0_), channel_id=1, source_target_pairs={{0,8},{1,3},{2,10},{3,1},{4,12},{5,7},{6,14},{7,5},{8,0},{9,11},{1... | collective-permute-start | bytes 442376 | tf_op jit(solution)/shard_map/ppermute | solution.py:261
  20.0 0.6 collective-permute-start.3
  20.6 0.6 collective-permute-start.2
  21.2 0.6 shard_map.98.near_ref
  21.8 1.8 %collective-permute-start.8 = (bf16[2,9,32,128]{3,2,1,0:T(8,128)(2,1)S(1)}, bf16[2,9,32,128]{3,2,1,0:T(8,128)(2,1)S(1)}, u32[]{:S(2)}, u32[]{:S(2)}) collective-permute-start(bf16[2,9,32,128]{3,2,1,0:T(8,128)(2,1)S(1)} %shard_map.97.refs_0_), channel_id=1, source_target_pairs={{0,14},{1,15},{2,12},{3,13},{4,10},{5,11},{6,8},{7,9},{8,6},{9,7},... | collective-permute-start | bytes 442376 | tf_op jit(solution)/shard_map/ppermute | solution.py:261
  23.6 0.6 collective-permute-done.4.refs_4_
  24.2 2.5 %collective-permute-done.3.refs_2_ = bf16[2,9,32,128]{3,2,1,0:T(8,128)(2,1)S(1)} collective-permute-done((bf16[2,9,32,128]{3,2,1,0:T(8,128)(2,1)S(1)}, bf16[2,9,32,128]{3,2,1,0:T(8,128)(2,1)S(1)}, u32[]{:S(2)}, u32[]{:S(2)}) %collective-permute-start.3) | collective-permute-done | bytes 147488 | tf_op jit(solution)/shard_map/ppermute | solution.py:261
  26.8 2.9 %collective-permute-done.2.refs_1_ = bf16[2,9,32,128]{3,2,1,0:T(8,128)(2,1)S(1)} collective-permute-done((bf16[2,9,32,128]{3,2,1,0:T(8,128)(2,1)S(1)}, bf16[2,9,32,128]{3,2,1,0:T(8,128)(2,1)S(1)}, u32[]{:S(2)}, u32[]{:S(2)}) %collective-permute-start.2) | collective-permute-done | bytes 147488 | tf_op jit(solution)/shard_map/ppermute | solution.py:261
  29.7 0.9 collective-permute-start.5
  31.1 3.7 %collective-permute-done.5.refs_3_ = bf16[2,9,32,128]{3,2,1,0:T(8,128)(2,1)S(1)} collective-permute-done((bf16[2,9,32,128]{3,2,1,0:T(8,128)(2,1)S(1)}, bf16[2,9,32,128]{3,2,1,0:T(8,128)(2,1)S(1)}, u32[]{:S(2)}, u32[]{:S(2)}) %collective-permute-start.5) | collective-permute-done | bytes 147488 | tf_op jit(solution)/shard_map/ppermute | solution.py:261
  34.8 0.9 collective-permute-done.7.refs_6_
  38.1 3.6 %shard_map.100 = (bf16[4,2,9,32,128]{4,3,2,1,0:T(8,128)(2,1)S(1)}, bf16[4,2,9,32,128]{4,3,2,1,0:T(8,128)(2,1)S(1)}, bf16[4,2,9,32,128]{4,3,2,1,0:T(8,128)(2,1)S(1)}, bf16[4,2,9,32,128]{4,3,2,1,0:T(8,128)(2,1)S(1)}) custom-call(s32[128]{0:T(128)S(1)} %bitcast.4, s32[128]{0:T(128)S(1)} %bitcast.6, bf16[128,96,96]{2,1,0:T(8,128)(2,1)S(1)} %copy-done.1, ...), custom_call_target="tpu_custom_call" | custom-call | flops 75497472 | bytes 10485760 | tf_op jit(solution)/shard_map/pallas_call | solution.py:403
  42.0 1.8 %collective-permute-done.17.swap_ref = bf16[4,2,9,32,128]{4,3,2,1,0:T(8,128)(2,1)S(1)} collective-permute-done((bf16[4,2,9,32,128]{4,3,2,1,0:T(8,128)(2,1)S(1)}, bf16[4,2,9,32,128]{4,3,2,1,0:T(8,128)(2,1)S(1)}, u32[]{:S(2)}, u32[]{:S(2)}) %collective-permute-start.17) | collective-permute-done | bytes 589856 | tf_op jit(solution)/shard_map/ppermute | solution.py:266
  44.2 1.2 collective-permute-start.18
  45.4 1.7 %collective-permute-start.19 = (bf16[2,9,32,128]{3,2,1,0:T(8,128)(2,1)S(1)}, bf16[2,9,32,128]{3,2,1,0:T(8,128)(2,1)S(1)}, u32[]{:S(2)}, u32[]{:S(2)}) collective-permute-start(bf16[2,9,32,128]{3,2,1,0:T(8,128)(2,1)S(1)} %get-tuple-element.139), channel_id=1, source_target_pairs={{0,8},{1,3},{2,10},{3,1},{4,12},{5,7},{6,14},{7,5},{8,0},{9,11},{1... | collective-permute-start | bytes 442376 | tf_op jit(solution)/shard_map/ppermute | solution.py:261
  47.7 2.5 %collective-permute-done.18.refs_0_ = bf16[2,9,32,128]{3,2,1,0:T(8,128)(2,1)S(1)} collective-permute-done((bf16[2,9,32,128]{3,2,1,0:T(8,128)(2,1)S(1)}, bf16[2,9,32,128]{3,2,1,0:T(8,128)(2,1)S(1)}, u32[]{:S(2)}, u32[]{:S(2)}) %collective-permute-start.18) | collective-permute-done | bytes 147488 | tf_op jit(solution)/shard_map/ppermute | solution.py:261
  50.2 1.0 collective-permute-done.19.refs_1_
  51.2 2.2 %collective-permute-done.20.refs_2_ = bf16[2,9,32,128]{3,2,1,0:T(8,128)(2,1)S(1)} collective-permute-done((bf16[2,9,32,128]{3,2,1,0:T(8,128)(2,1)S(1)}, bf16[2,9,32,128]{3,2,1,0:T(8,128)(2,1)S(1)}, u32[]{:S(2)}, u32[]{:S(2)}) %collective-permute-start.20) | collective-permute-done | bytes 147488 | tf_op jit(solution)/shard_map/ppermute | solution.py:261
  53.5 0.6 collective-permute-done.21.refs_3_
  54.4 1.2 collective-permute-start.23
  55.6 0.9 collective-permute-start.24
  56.5 0.9 collective-permute-start.25
  57.8 0.7 collective-permute-done.26.inner_ref
  58.8 1.5 %collective-permute-done.23.refs_0_ = bf16[2,9,32,128]{3,2,1,0:T(8,128)(2,1)S(1)} collective-permute-done((bf16[2,9,32,128]{3,2,1,0:T(8,128)(2,1)S(1)}, bf16[2,9,32,128]{3,2,1,0:T(8,128)(2,1)S(1)}, u32[]{:S(2)}, u32[]{:S(2)}) %collective-permute-start.23) | collective-permute-done | bytes 147488 | tf_op jit(solution)/shard_map/ppermute | solution.py:261
  60.7 0.9 collective-permute-done.25.refs_2_
  61.7 0.7 collective-permute-start.28
  62.4 5.4 %collective-permute-done.28.rest_0_ = bf16[9,32,128]{2,1,0:T(8,128)(2,1)S(1)} collective-permute-done((bf16[9,32,128]{2,1,0:T(8,128)(2,1)S(1)}, bf16[9,32,128]{2,1,0:T(8,128)(2,1)S(1)}, u32[]{:S(2)}, u32[]{:S(2)}) %collective-permute-start.28) | collective-permute-done | bytes 73760 | tf_op jit(solution)/shard_map/ppermute | solution.py:257
  67.8 1.6 %shard_map.105 = (bf16[8,32,256]{2,1,0:T(8,128)(2,1)}, bf16[9,32,128]{2,1,0:T(8,128)(2,1)S(1)}, bf16[1,32,256]{2,1,0:T(8,128)(2,1)S(1)}, bf16[1,32,256]{2,1,0:T(8,128)(2,1)S(1)}) custom-call(s32[12]{0:T(128)S(1)} %copy-done.8, f32[8,32,256]{2,1,0:T(8,128)S(1)} %shard_map.98.near_ref, f32[2,32,256]{2,1,0:T(8,128)S(1)} %shard_map.103.edge_ref, ...), custom_call_target="tpu_custom_call" | custom-call | tf_op jit(solution)/shard_map/pallas_call | solution.py:423
  69.4 5.6 %collective-permute-done.29.refs_1_ = bf16[9,32,128]{2,1,0:T(8,128)(2,1)S(1)} collective-permute-done((bf16[9,32,128]{2,1,0:T(8,128)(2,1)S(1)}, bf16[9,32,128]{2,1,0:T(8,128)(2,1)S(1)}, u32[]{:S(2)}, u32[]{:S(2)}) %collective-permute-start.29) | collective-permute-done | bytes 73760 | tf_op jit(solution)/shard_map/ppermute | solution.py:257
  75.1 1.0 collective-permute-start.31
  76.1 1.5 %collective-permute-start.30 = (bf16[2,9,32,128]{3,2,1,0:T(8,128)(2,1)S(1)}, bf16[2,9,32,128]{3,2,1,0:T(8,128)(2,1)S(1)}, u32[]{:S(2)}, u32[]{:S(2)}) collective-permute-start(bf16[2,9,32,128]{3,2,1,0:T(8,128)(2,1)S(1)} %shard_map.106.refs_0_), channel_id=1, source_target_pairs={{0,2},{1,5},{2,0},{3,7},{4,6},{5,1},{6,4},{7,3},{8,10},{9,13},{10,... | collective-permute-start | bytes 442376 | tf_op jit(solution)/shard_map/ppermute | solution.py:261
  77.7 0.9 copy-done.6
  78.6 0.6 shard_map.107.near_ref
  79.2 2.4 %collective-permute-start.36 = (bf16[2,9,32,128]{3,2,1,0:T(8,128)(2,1)S(1)}, bf16[2,9,32,128]{3,2,1,0:T(8,128)(2,1)S(1)}, u32[]{:S(2)}, u32[]{:S(2)}) collective-permute-start(bf16[2,9,32,128]{3,2,1,0:T(8,128)(2,1)S(1)} %shard_map.106.refs_0_), channel_id=1, source_target_pairs={{0,14},{1,15},{2,12},{3,13},{4,10},{5,11},{6,8},{7,9},{8,6},{9,7},... | collective-permute-start | bytes 442376 | tf_op jit(solution)/shard_map/ppermute | solution.py:261
  81.8 0.9 collective-permute-done.30.refs_1_
  82.6 1.2 collective-permute-start.33
  83.8 1.3 %collective-permute-start.37 = (bf16[1,32,256]{2,1,0:T(8,128)(2,1)S(1)}, bf16[1,32,256]{2,1,0:T(8,128)(2,1)S(1)}, u32[]{:S(2)}, u32[]{:S(2)}) collective-permute-start(bf16[1,32,256]{2,1,0:T(8,128)(2,1)S(1)} %get-tuple-element.174), channel_id=1, source_target_pairs={{1,3},{3,5},{5,7},{7,9},{9,11},{11,13},{13,15},{15,17},{17,19},{19... | collective-permute-start | bytes 49160 | tf_op jit(solution)/shard_map/ppermute | solution.py:399
  85.1 3.4 %collective-permute-start.35 = (bf16[2,9,32,128]{3,2,1,0:T(8,128)(2,1)S(1)}, bf16[2,9,32,128]{3,2,1,0:T(8,128)(2,1)S(1)}, u32[]{:S(2)}, u32[]{:S(2)}) collective-permute-start(bf16[2,9,32,128]{3,2,1,0:T(8,128)(2,1)S(1)} %collective-permute-done.31.refs_2_), channel_id=1, source_target_pairs={{0,8},{1,3},{2,10},{3,1},{4,12},{5,7},{6,14},{7,5},{8,0},{9,11},{1... | collective-permute-start | bytes 442376 | tf_op jit(solution)/shard_map/ppermute | solution.py:261
  88.5 0.9 collective-permute-start.34
  90.0 1.6 %collective-permute-done.35.refs_6_ = bf16[2,9,32,128]{3,2,1,0:T(8,128)(2,1)S(1)} collective-permute-done((bf16[2,9,32,128]{3,2,1,0:T(8,128)(2,1)S(1)}, bf16[2,9,32,128]{3,2,1,0:T(8,128)(2,1)S(1)}, u32[]{:S(2)}, u32[]{:S(2)}) %collective-permute-start.35) | collective-permute-done | bytes 147488 | tf_op jit(solution)/shard_map/ppermute | solution.py:261
  91.7 1.9 %collective-permute-done.34.refs_5_ = bf16[2,9,32,128]{3,2,1,0:T(8,128)(2,1)S(1)} collective-permute-done((bf16[2,9,32,128]{3,2,1,0:T(8,128)(2,1)S(1)}, bf16[2,9,32,128]{3,2,1,0:T(8,128)(2,1)S(1)}, u32[]{:S(2)}, u32[]{:S(2)}) %collective-permute-start.34) | collective-permute-done | bytes 147488 | tf_op jit(solution)/shard_map/ppermute | solution.py:261
  95.7 3.6 %shard_map.108 = (bf16[4,2,9,32,128]{4,3,2,1,0:T(8,128)(2,1)S(1)}, bf16[4,2,9,32,128]{4,3,2,1,0:T(8,128)(2,1)S(1)}, bf16[4,2,9,32,128]{4,3,2,1,0:T(8,128)(2,1)S(1)}, bf16[4,2,9,32,128]{4,3,2,1,0:T(8,128)(2,1)S(1)}) custom-call(s32[128]{0:T(128)S(1)} %bitcast.5, s32[128]{0:T(128)S(1)} %bitcast.7, bf16[128,96,96]{2,1,0:T(8,128)(2,1)S(1)} %copy-done.1, ...), custom_call_target="tpu_custom_call" | custom-call | flops 75497472 | bytes 10485760 | tf_op jit(solution)/shard_map/pallas_call | solution.py:403
  99.7 1.7 %collective-permute-done.46.swap_ref = bf16[4,2,9,32,128]{4,3,2,1,0:T(8,128)(2,1)S(1)} collective-permute-done((bf16[4,2,9,32,128]{4,3,2,1,0:T(8,128)(2,1)S(1)}, bf16[4,2,9,32,128]{4,3,2,1,0:T(8,128)(2,1)S(1)}, u32[]{:S(2)}, u32[]{:S(2)}) %collective-permute-start.46) | collective-permute-done | bytes 589856 | tf_op jit(solution)/shard_map/ppermute | solution.py:266
  101.9 0.8 collective-permute-start.47
  102.7 1.1 collective-permute-start.48
  104.3 2.0 %collective-permute-start.50 = (bf16[2,9,32,128]{3,2,1,0:T(8,128)(2,1)S(1)}, bf16[2,9,32,128]{3,2,1,0:T(8,128)(2,1)S(1)}, u32[]{:S(2)}, u32[]{:S(2)}) collective-permute-start(bf16[2,9,32,128]{3,2,1,0:T(8,128)(2,1)S(1)} %get-tuple-element.194), channel_id=1, source_target_pairs={{0,12},{1,11},{2,14},{3,9},{4,8},{5,15},{6,10},{7,13},{8,4},{9,3},... | collective-permute-start | bytes 442376 | tf_op jit(solution)/shard_map/ppermute | solution.py:261
  106.3 2.2 %collective-permute-done.47.refs_0_ = bf16[2,9,32,128]{3,2,1,0:T(8,128)(2,1)S(1)} collective-permute-done((bf16[2,9,32,128]{3,2,1,0:T(8,128)(2,1)S(1)}, bf16[2,9,32,128]{3,2,1,0:T(8,128)(2,1)S(1)}, u32[]{:S(2)}, u32[]{:S(2)}) %collective-permute-start.47) | collective-permute-done | bytes 147488 | tf_op jit(solution)/shard_map/ppermute | solution.py:261
  108.6 1.9 %collective-permute-done.49.refs_2_ = bf16[2,9,32,128]{3,2,1,0:T(8,128)(2,1)S(1)} collective-permute-done((bf16[2,9,32,128]{3,2,1,0:T(8,128)(2,1)S(1)}, bf16[2,9,32,128]{3,2,1,0:T(8,128)(2,1)S(1)}, u32[]{:S(2)}, u32[]{:S(2)}) %collective-permute-start.49) | collective-permute-done | bytes 147488 | tf_op jit(solution)/shard_map/ppermute | solution.py:261
  110.4 1.2 collective-permute-done.50.refs_3_
  111.9 1.0 collective-permute-start.52
  112.9 1.2 collective-permute-start.53
  115.0 0.7 collective-permute-done.55.inner_ref
  116.0 1.4 %collective-permute-done.52.refs_0_ = bf16[2,9,32,128]{3,2,1,0:T(8,128)(2,1)S(1)} collective-permute-done((bf16[2,9,32,128]{3,2,1,0:T(8,128)(2,1)S(1)}, bf16[2,9,32,128]{3,2,1,0:T(8,128)(2,1)S(1)}, u32[]{:S(2)}, u32[]{:S(2)}) %collective-permute-start.52) | collective-permute-done | bytes 147488 | tf_op jit(solution)/shard_map/ppermute | solution.py:261
  117.3 0.7 collective-permute-done.53.refs_1_
  118.1 1.2 collective-permute-done.54.refs_2_
  119.4 0.8 collective-permute-start.57
  120.2 5.1 %collective-permute-done.57.rest_0_ = bf16[9,32,128]{2,1,0:T(8,128)(2,1)S(1)} collective-permute-done((bf16[9,32,128]{2,1,0:T(8,128)(2,1)S(1)}, bf16[9,32,128]{2,1,0:T(8,128)(2,1)S(1)}, u32[]{:S(2)}, u32[]{:S(2)}) %collective-permute-start.57) | collective-permute-done | bytes 73760 | tf_op jit(solution)/shard_map/ppermute | solution.py:257
  125.2 1.6 %shard_map.113 = bf16[8,32,256]{2,1,0:T(8,128)(2,1)} custom-call(s32[12]{0:T(128)S(1)} %copy-done.8, f32[8,32,256]{2,1,0:T(8,128)S(1)} %shard_map.107.near_ref, f32[2,32,256]{2,1,0:T(8,128)S(1)} %shard_map.111.edge_ref, bf16[8,96,256]{2,1,0:T(8,128)(2,1)S(1)} %copy-done.2, bf16[8,96,96]{2,1,0:T(8,128)(2,1)S(1)} %copy-done.3, ...), custom_call_target="tpu_custom_call" | custom-call | tf_op jit(solution)/shard_map/pallas_call | solution.py:423
  (96 shorter events, 11.6 us)
Async XLA Ops:
  3.5 11.0 %collective-permute-start.1 = (bf16[9,32,128]{2,1,0:T(8,128)(2,1)}, bf16[9,32,128]{2,1,0:T(8,128)(2,1)S(1)}, u32[]{:S(2)}, u32[]{:S(2)}) collective-permute-start(bf16[9,32,128]{2,1,0:T(8,128)(2,1)} %get-tuple-element.111.__.refs_0_), channel_id=1, source_target_pairs={{0,16},{1,17},{2,18},{3,19},{4,20},{5,21},{6,22},{7,23},{8,24},{9,... | collective-permute-start | bytes 221192 | tf_op jit(solution)/shard_map/ppermute | solution.py:257
  7.6 13.6 %copy-start = (bf16[8,3,256,256]{3,2,1,0:T(8,128)(2,1)S(1)}, bf16[8,3,256,256]{3,2,1,0:T(8,128)(2,1)}, u32[]{:S(2)}) copy-start(bf16[8,3,256,256]{3,2,1,0:T(8,128)(2,1)} %last_ref.3) | copy-start | bytes 9437188
  7.6 13.6 %copy-start.4 = (bf16[8,32,256]{2,1,0:T(8,128)(2,1)S(1)}, bf16[8,32,256]{2,1,0:T(8,128)(2,1)}, u32[]{:S(2)}) copy-start(bf16[8,32,256]{2,1,0:T(8,128)(2,1)} %v_ref.1) | copy-start | bytes 393220
  7.6 6.9 %collective-permute-start = (bf16[1,32,256]{2,1,0:T(8,128)(2,1)}, bf16[1,32,256]{2,1,0:T(8,128)(2,1)S(1)}, u32[]{:S(2)}, u32[]{:S(2)}) collective-permute-start(bf16[1,32,256]{2,1,0:T(8,128)(2,1)} %get-tuple-element.112), channel_id=1, source_target_pairs={{1,3},{3,5},{5,7},{7,9},{9,11},{11,13},{13,15},{15,17},{17,19},{19... | collective-permute-start | bytes 49160 | tf_op jit(solution)/shard_map/ppermute | solution.py:388
  14.0 22.9 %copy-start.9 = (s32[128]{0:T(128)S(1)}, s32[128]{0:T(128)}, u32[]{:S(2)}) copy-start(s32[128]{0:T(128)} %param.14) | copy-start | bytes 1540
  14.0 22.9 %copy-start.10 = (s32[128]{0:T(128)S(1)}, s32[128]{0:T(128)}, u32[]{:S(2)}) copy-start(s32[128]{0:T(128)} %param.15) | copy-start | bytes 1540
  14.6 23.6 %copy-start.1 = (bf16[128,96,96]{2,1,0:T(8,128)(2,1)S(1)}, bf16[128,96,96]{2,1,0:T(8,128)(2,1)}, u32[]{:S(2)}) copy-start(bf16[128,96,96]{2,1,0:T(8,128)(2,1)} %copy.10._.coupling_ref) | copy-start | bytes 7077892
  15.4 8.8 %collective-permute-start.4 = (bf16[2,9,32,128]{3,2,1,0:T(8,128)(2,1)S(1)}, bf16[2,9,32,128]{3,2,1,0:T(8,128)(2,1)S(1)}, u32[]{:S(2)}, u32[]{:S(2)}) collective-permute-start(bf16[2,9,32,128]{3,2,1,0:T(8,128)(2,1)S(1)} %shard_map.97.refs_0_), channel_id=1, source_target_pairs={{0,8},{1,3},{2,10},{3,1},{4,12},{5,7},{6,14},{7,5},{8,0},{9,11},{1... | collective-permute-start | bytes 442376 | tf_op jit(solution)/shard_map/ppermute | solution.py:261
  20.0 6.7 %collective-permute-start.3 = (bf16[2,9,32,128]{3,2,1,0:T(8,128)(2,1)S(1)}, bf16[2,9,32,128]{3,2,1,0:T(8,128)(2,1)S(1)}, u32[]{:S(2)}, u32[]{:S(2)}) collective-permute-start(bf16[2,9,32,128]{3,2,1,0:T(8,128)(2,1)S(1)} %shard_map.97.refs_0_), channel_id=1, source_target_pairs={{0,4},{1,9},{2,6},{3,11},{4,0},{5,13},{6,2},{7,15},{8,12},{9,1},{1... | collective-permute-start | bytes 442376 | tf_op jit(solution)/shard_map/ppermute | solution.py:261
  20.6 9.0 %collective-permute-start.2 = (bf16[2,9,32,128]{3,2,1,0:T(8,128)(2,1)S(1)}, bf16[2,9,32,128]{3,2,1,0:T(8,128)(2,1)S(1)}, u32[]{:S(2)}, u32[]{:S(2)}) collective-permute-start(bf16[2,9,32,128]{3,2,1,0:T(8,128)(2,1)S(1)} %shard_map.97.refs_0_), channel_id=1, source_target_pairs={{0,2},{1,5},{2,0},{3,7},{4,6},{5,1},{6,4},{7,3},{8,10},{9,13},{10,... | collective-permute-start | bytes 442376 | tf_op jit(solution)/shard_map/ppermute | solution.py:261
  21.8 8.8 %collective-permute-start.8 = (bf16[2,9,32,128]{3,2,1,0:T(8,128)(2,1)S(1)}, bf16[2,9,32,128]{3,2,1,0:T(8,128)(2,1)S(1)}, u32[]{:S(2)}, u32[]{:S(2)}) collective-permute-start(bf16[2,9,32,128]{3,2,1,0:T(8,128)(2,1)S(1)} %shard_map.97.refs_0_), channel_id=1, source_target_pairs={{0,14},{1,15},{2,12},{3,13},{4,10},{5,11},{6,8},{7,9},{8,6},{9,7},... | collective-permute-start | bytes 442376 | tf_op jit(solution)/shard_map/ppermute | solution.py:261
  29.7 5.1 %collective-permute-start.5 = (bf16[2,9,32,128]{3,2,1,0:T(8,128)(2,1)S(1)}, bf16[2,9,32,128]{3,2,1,0:T(8,128)(2,1)S(1)}, u32[]{:S(2)}, u32[]{:S(2)}) collective-permute-start(bf16[2,9,32,128]{3,2,1,0:T(8,128)(2,1)S(1)} %collective-permute-done.2.refs_1_), channel_id=1, source_target_pairs={{0,4},{1,9},{2,6},{3,11},{4,0},{5,13},{6,2},{7,15},{8,12},{9,1},{1... | collective-permute-start | bytes 442376 | tf_op jit(solution)/shard_map/ppermute | solution.py:261
  30.6 5.1 %collective-permute-start.7 = (bf16[2,9,32,128]{3,2,1,0:T(8,128)(2,1)S(1)}, bf16[2,9,32,128]{3,2,1,0:T(8,128)(2,1)S(1)}, u32[]{:S(2)}, u32[]{:S(2)}) collective-permute-start(bf16[2,9,32,128]{3,2,1,0:T(8,128)(2,1)S(1)} %collective-permute-done.3.refs_2_), channel_id=1, source_target_pairs={{0,8},{1,3},{2,10},{3,1},{4,12},{5,7},{6,14},{7,5},{8,0},{9,11},{1... | collective-permute-start | bytes 442376 | tf_op jit(solution)/shard_map/ppermute | solution.py:261
  30.6 5.1 %collective-permute-start.6 = (bf16[2,9,32,128]{3,2,1,0:T(8,128)(2,1)S(1)}, bf16[2,9,32,128]{3,2,1,0:T(8,128)(2,1)S(1)}, u32[]{:S(2)}, u32[]{:S(2)}) collective-permute-start(bf16[2,9,32,128]{3,2,1,0:T(8,128)(2,1)S(1)} %collective-permute-done.4.refs_4_), channel_id=1, source_target_pairs={{0,2},{1,5},{2,0},{3,7},{4,6},{5,1},{6,4},{7,3},{8,10},{9,13},{10,... | collective-permute-start | bytes 442376 | tf_op jit(solution)/shard_map/ppermute | solution.py:261
  30.6 5.7 %collective-permute-start.9 = (bf16[2,9,32,128]{3,2,1,0:T(8,128)(2,1)S(1)}, bf16[2,9,32,128]{3,2,1,0:T(8,128)(2,1)S(1)}, u32[]{:S(2)}, u32[]{:S(2)}) collective-permute-start(bf16[2,9,32,128]{3,2,1,0:T(8,128)(2,1)S(1)} %shard_map.97.refs_0_), channel_id=1, source_target_pairs={{0,1},{1,0},{2,3},{3,2},{4,5},{5,4},{6,7},{7,6},{8,9},{9,8},{10,11... | collective-permute-start | bytes 442376 | tf_op jit(solution)/shard_map/ppermute | solution.py:266
  30.6 5.7 %collective-permute-start.10 = (bf16[2,9,32,128]{3,2,1,0:T(8,128)(2,1)S(1)}, bf16[2,9,32,128]{3,2,1,0:T(8,128)(2,1)S(1)}, u32[]{:S(2)}, u32[]{:S(2)}) collective-permute-start(bf16[2,9,32,128]{3,2,1,0:T(8,128)(2,1)S(1)} %collective-permute-done.2.refs_1_), channel_id=1, source_target_pairs={{0,1},{1,0},{2,3},{3,2},{4,5},{5,4},{6,7},{7,6},{8,9},{9,8},{10,11... | collective-permute-start | bytes 442376 | tf_op jit(solution)/shard_map/ppermute | solution.py:266
  34.8 2.0 %collective-permute-start.11 = (bf16[2,9,32,128]{3,2,1,0:T(8,128)(2,1)S(1)}, bf16[2,9,32,128]{3,2,1,0:T(8,128)(2,1)S(1)}, u32[]{:S(2)}, u32[]{:S(2)}) collective-permute-start(bf16[2,9,32,128]{3,2,1,0:T(8,128)(2,1)S(1)} %collective-permute-done.3.refs_2_), channel_id=1, source_target_pairs={{0,1},{1,0},{2,3},{3,2},{4,5},{5,4},{6,7},{7,6},{8,9},{9,8},{10,11... | collective-permute-start | bytes 442376 | tf_op jit(solution)/shard_map/ppermute | solution.py:266
  35.7 1.4 %collective-permute-start.13 = (bf16[2,9,32,128]{3,2,1,0:T(8,128)(2,1)S(1)}, bf16[2,9,32,128]{3,2,1,0:T(8,128)(2,1)S(1)}, u32[]{:S(2)}, u32[]{:S(2)}) collective-permute-start(bf16[2,9,32,128]{3,2,1,0:T(8,128)(2,1)S(1)} %collective-permute-done.4.refs_4_), channel_id=1, source_target_pairs={{0,1},{1,0},{2,3},{3,2},{4,5},{5,4},{6,7},{7,6},{8,9},{9,8},{10,11... | collective-permute-start | bytes 442376 | tf_op jit(solution)/shard_map/ppermute | solution.py:266
  35.7 1.6 %collective-permute-start.12 = (bf16[2,9,32,128]{3,2,1,0:T(8,128)(2,1)S(1)}, bf16[2,9,32,128]{3,2,1,0:T(8,128)(2,1)S(1)}, u32[]{:S(2)}, u32[]{:S(2)}) collective-permute-start(bf16[2,9,32,128]{3,2,1,0:T(8,128)(2,1)S(1)} %collective-permute-done.5.refs_3_), channel_id=1, source_target_pairs={{0,1},{1,0},{2,3},{3,2},{4,5},{5,4},{6,7},{7,6},{8,9},{9,8},{10,11... | collective-permute-start | bytes 442376 | tf_op jit(solution)/shard_map/ppermute | solution.py:266
  36.3 1.4 %collective-permute-start.14 = (bf16[2,9,32,128]{3,2,1,0:T(8,128)(2,1)S(1)}, bf16[2,9,32,128]{3,2,1,0:T(8,128)(2,1)S(1)}, u32[]{:S(2)}, u32[]{:S(2)}) collective-permute-start(bf16[2,9,32,128]{3,2,1,0:T(8,128)(2,1)S(1)} %collective-permute-done.6.refs_5_), channel_id=1, source_target_pairs={{0,1},{1,0},{2,3},{3,2},{4,5},{5,4},{6,7},{7,6},{8,9},{9,8},{10,11... | collective-permute-start | bytes 442376 | tf_op jit(solution)/shard_map/ppermute | solution.py:266
  36.3 1.5 %collective-permute-start.15 = (bf16[2,9,32,128]{3,2,1,0:T(8,128)(2,1)S(1)}, bf16[2,9,32,128]{3,2,1,0:T(8,128)(2,1)S(1)}, u32[]{:S(2)}, u32[]{:S(2)}) collective-permute-start(bf16[2,9,32,128]{3,2,1,0:T(8,128)(2,1)S(1)} %collective-permute-done.7.refs_6_), channel_id=1, source_target_pairs={{0,1},{1,0},{2,3},{3,2},{4,5},{5,4},{6,7},{7,6},{8,9},{9,8},{10,11... | collective-permute-start | bytes 442376 | tf_op jit(solution)/shard_map/ppermute | solution.py:266
  36.8 1.4 %collective-permute-start.16 = (bf16[2,9,32,128]{3,2,1,0:T(8,128)(2,1)S(1)}, bf16[2,9,32,128]{3,2,1,0:T(8,128)(2,1)S(1)}, u32[]{:S(2)}, u32[]{:S(2)}) collective-permute-start(bf16[2,9,32,128]{3,2,1,0:T(8,128)(2,1)S(1)} %collective-permute-done.8.refs_7_), channel_id=1, source_target_pairs={{0,1},{1,0},{2,3},{3,2},{4,5},{5,4},{6,7},{7,6},{8,9},{9,8},{10,11... | collective-permute-start | bytes 442376 | tf_op jit(solution)/shard_map/ppermute | solution.py:266
  38.1 19.2 %copy-start.11 = (bf16[1,32,256]{2,1,0:T(8,128)(2,1)S(1)}, bf16[1,32,256]{2,1,0:T(8,128)(2,1)}, u32[]{:S(2)}) copy-start(bf16[1,32,256]{2,1,0:T(8,128)(2,1)} %get-tuple-element.158) | copy-start | bytes 49156
  41.8 2.1 %collective-permute-start.17 = (bf16[4,2,9,32,128]{4,3,2,1,0:T(8,128)(2,1)S(1)}, bf16[4,2,9,32,128]{4,3,2,1,0:T(8,128)(2,1)S(1)}, u32[]{:S(2)}, u32[]{:S(2)}) collective-permute-start(bf16[4,2,9,32,128]{4,3,2,1,0:T(8,128)(2,1)S(1)} %get-tuple-element.132), channel_id=1, source_target_pairs={{0,1},{1,0},{2,3},{3,2},{4,5},{5,4},{6,7},{7,6},{8,9},{9,8},{10,11... | collective-permute-start | bytes 1769480 | tf_op jit(solution)/shard_map/ppermute | solution.py:266
  44.0 10.1 %collective-permute-start.22 = (bf16[4,2,9,32,128]{4,3,2,1,0:T(8,128)(2,1)S(1)}, bf16[4,2,9,32,128]{4,3,2,1,0:T(8,128)(2,1)S(1)}, u32[]{:S(2)}, u32[]{:S(2)}) collective-permute-start(bf16[4,2,9,32,128]{4,3,2,1,0:T(8,128)(2,1)S(1)} %get-tuple-element.142), channel_id=1, source_target_pairs={{0,1},{1,0},{2,3},{3,2},{4,5},{5,4},{6,7},{7,6},{8,9},{9,8},{10,11... | collective-permute-start | bytes 1769480 | tf_op jit(solution)/shard_map/ppermute | solution.py:266
  44.2 6.0 %collective-permute-start.18 = (bf16[2,9,32,128]{3,2,1,0:T(8,128)(2,1)S(1)}, bf16[2,9,32,128]{3,2,1,0:T(8,128)(2,1)S(1)}, u32[]{:S(2)}, u32[]{:S(2)}) collective-permute-start(bf16[2,9,32,128]{3,2,1,0:T(8,128)(2,1)S(1)} %get-tuple-element.138), channel_id=1, source_target_pairs={{0,4},{1,9},{2,6},{3,11},{4,0},{5,13},{6,2},{7,15},{8,12},{9,1},{1... | collective-permute-start | bytes 442376 | tf_op jit(solution)/shard_map/ppermute | solution.py:261
  45.4 5.8 %collective-permute-start.19 = (bf16[2,9,32,128]{3,2,1,0:T(8,128)(2,1)S(1)}, bf16[2,9,32,128]{3,2,1,0:T(8,128)(2,1)S(1)}, u32[]{:S(2)}, u32[]{:S(2)}) collective-permute-start(bf16[2,9,32,128]{3,2,1,0:T(8,128)(2,1)S(1)} %get-tuple-element.139), channel_id=1, source_target_pairs={{0,8},{1,3},{2,10},{3,1},{4,12},{5,7},{6,14},{7,5},{8,0},{9,11},{1... | collective-permute-start | bytes 442376 | tf_op jit(solution)/shard_map/ppermute | solution.py:261
  47.2 6.3 %collective-permute-start.20 = (bf16[2,9,32,128]{3,2,1,0:T(8,128)(2,1)S(1)}, bf16[2,9,32,128]{3,2,1,0:T(8,128)(2,1)S(1)}, u32[]{:S(2)}, u32[]{:S(2)}) collective-permute-start(bf16[2,9,32,128]{3,2,1,0:T(8,128)(2,1)S(1)} %get-tuple-element.140), channel_id=1, source_target_pairs={{0,2},{1,5},{2,0},{3,7},{4,6},{5,1},{6,4},{7,3},{8,10},{9,13},{10,... | collective-permute-start | bytes 442376 | tf_op jit(solution)/shard_map/ppermute | solution.py:261
  47.2 6.9 %collective-permute-start.21 = (bf16[2,9,32,128]{3,2,1,0:T(8,128)(2,1)S(1)}, bf16[2,9,32,128]{3,2,1,0:T(8,128)(2,1)S(1)}, u32[]{:S(2)}, u32[]{:S(2)}) collective-permute-start(bf16[2,9,32,128]{3,2,1,0:T(8,128)(2,1)S(1)} %get-tuple-element.141), channel_id=1, source_target_pairs={{0,12},{1,11},{2,14},{3,9},{4,8},{5,15},{6,10},{7,13},{8,4},{9,3},... | collective-permute-start | bytes 442376 | tf_op jit(solution)/shard_map/ppermute | solution.py:261
  54.4 6.0 %collective-permute-start.23 = (bf16[2,9,32,128]{3,2,1,0:T(8,128)(2,1)S(1)}, bf16[2,9,32,128]{3,2,1,0:T(8,128)(2,1)S(1)}, u32[]{:S(2)}, u32[]{:S(2)}) collective-permute-start(bf16[2,9,32,128]{3,2,1,0:T(8,128)(2,1)S(1)} %get-tuple-element.155), channel_id=1, source_target_pairs={{0,2},{1,5},{2,0},{3,7},{4,6},{5,1},{6,4},{7,3},{8,10},{9,13},{10,... | collective-permute-start | bytes 442376 | tf_op jit(solution)/shard_map/ppermute | solution.py:261
  55.6 5.1 %collective-permute-start.24 = (bf16[2,9,32,128]{3,2,1,0:T(8,128)(2,1)S(1)}, bf16[2,9,32,128]{3,2,1,0:T(8,128)(2,1)S(1)}, u32[]{:S(2)}, u32[]{:S(2)}) collective-permute-start(bf16[2,9,32,128]{3,2,1,0:T(8,128)(2,1)S(1)} %get-tuple-element.156), channel_id=1, source_target_pairs={{0,4},{1,9},{2,6},{3,11},{4,0},{5,13},{6,2},{7,15},{8,12},{9,1},{1... | collective-permute-start | bytes 442376 | tf_op jit(solution)/shard_map/ppermute | solution.py:261
  56.5 5.1 %collective-permute-start.25 = (bf16[2,9,32,128]{3,2,1,0:T(8,128)(2,1)S(1)}, bf16[2,9,32,128]{3,2,1,0:T(8,128)(2,1)S(1)}, u32[]{:S(2)}, u32[]{:S(2)}) collective-permute-start(bf16[2,9,32,128]{3,2,1,0:T(8,128)(2,1)S(1)} %get-tuple-element.157), channel_id=1, source_target_pairs={{0,8},{1,3},{2,10},{3,1},{4,12},{5,7},{6,14},{7,5},{8,0},{9,11},{1... | collective-permute-start | bytes 442376 | tf_op jit(solution)/shard_map/ppermute | solution.py:261
  57.3 1.2 collective-permute-start.26
  57.3 1.3 %collective-permute-start.27 = (bf16[1,32,256]{2,1,0:T(8,128)(2,1)S(1)}, bf16[1,32,256]{2,1,0:T(8,128)(2,1)S(1)}, u32[]{:S(2)}, u32[]{:S(2)}) collective-permute-start(bf16[1,32,256]{2,1,0:T(8,128)(2,1)S(1)} %collective-permute-done), channel_id=1, source_target_pairs={{0,1},{1,0},{2,3},{3,2},{4,5},{5,4},{6,7},{7,6},{8,9},{9,8},{10,11... | collective-permute-start | bytes 49160 | tf_op jit(solution)/shard_map/ppermute | solution.py:266
  61.7 6.1 %collective-permute-start.28 = (bf16[9,32,128]{2,1,0:T(8,128)(2,1)S(1)}, bf16[9,32,128]{2,1,0:T(8,128)(2,1)S(1)}, u32[]{:S(2)}, u32[]{:S(2)}) collective-permute-start(bf16[9,32,128]{2,1,0:T(8,128)(2,1)S(1)} %get-tuple-element.166), channel_id=1, source_target_pairs={{0,16},{1,17},{2,18},{3,19},{4,20},{5,21},{6,22},{7,23},{8,24},{9,... | collective-permute-start | bytes 221192 | tf_op jit(solution)/shard_map/ppermute | solution.py:257
  69.4 5.6 %collective-permute-start.29 = (bf16[9,32,128]{2,1,0:T(8,128)(2,1)S(1)}, bf16[9,32,128]{2,1,0:T(8,128)(2,1)S(1)}, u32[]{:S(2)}, u32[]{:S(2)}) collective-permute-start(bf16[9,32,128]{2,1,0:T(8,128)(2,1)S(1)} %get-tuple-element.168.refs_0_), channel_id=1, source_target_pairs={{0,16},{1,17},{2,18},{3,19},{4,20},{5,21},{6,22},{7,23},{8,24},{9,... | collective-permute-start | bytes 221192 | tf_op jit(solution)/shard_map/ppermute | solution.py:257
  75.1 6.7 %collective-permute-start.32 = (bf16[2,9,32,128]{3,2,1,0:T(8,128)(2,1)S(1)}, bf16[2,9,32,128]{3,2,1,0:T(8,128)(2,1)S(1)}, u32[]{:S(2)}, u32[]{:S(2)}) collective-permute-start(bf16[2,9,32,128]{3,2,1,0:T(8,128)(2,1)S(1)} %shard_map.106.refs_0_), channel_id=1, source_target_pairs={{0,8},{1,3},{2,10},{3,1},{4,12},{5,7},{6,14},{7,5},{8,0},{9,11},{1... | collective-permute-start | bytes 442376 | tf_op jit(solution)/shard_map/ppermute | solution.py:261
  75.1 6.6 %collective-permute-start.31 = (bf16[2,9,32,128]{3,2,1,0:T(8,128)(2,1)S(1)}, bf16[2,9,32,128]{3,2,1,0:T(8,128)(2,1)S(1)}, u32[]{:S(2)}, u32[]{:S(2)}) collective-permute-start(bf16[2,9,32,128]{3,2,1,0:T(8,128)(2,1)S(1)} %shard_map.106.refs_0_), channel_id=1, source_target_pairs={{0,4},{1,9},{2,6},{3,11},{4,0},{5,13},{6,2},{7,15},{8,12},{9,1},{1... | collective-permute-start | bytes 442376 | tf_op jit(solution)/shard_map/ppermute | solution.py:261
  76.1 6.5 %collective-permute-start.30 = (bf16[2,9,32,128]{3,2,1,0:T(8,128)(2,1)S(1)}, bf16[2,9,32,128]{3,2,1,0:T(8,128)(2,1)S(1)}, u32[]{:S(2)}, u32[]{:S(2)}) collective-permute-start(bf16[2,9,32,128]{3,2,1,0:T(8,128)(2,1)S(1)} %shard_map.106.refs_0_), channel_id=1, source_target_pairs={{0,2},{1,5},{2,0},{3,7},{4,6},{5,1},{6,4},{7,3},{8,10},{9,13},{10,... | collective-permute-start | bytes 442376 | tf_op jit(solution)/shard_map/ppermute | solution.py:261
  79.2 10.3 %collective-permute-start.36 = (bf16[2,9,32,128]{3,2,1,0:T(8,128)(2,1)S(1)}, bf16[2,9,32,128]{3,2,1,0:T(8,128)(2,1)S(1)}, u32[]{:S(2)}, u32[]{:S(2)}) collective-permute-start(bf16[2,9,32,128]{3,2,1,0:T(8,128)(2,1)S(1)} %shard_map.106.refs_0_), channel_id=1, source_target_pairs={{0,14},{1,15},{2,12},{3,13},{4,10},{5,11},{6,8},{7,9},{8,6},{9,7},... | collective-permute-start | bytes 442376 | tf_op jit(solution)/shard_map/ppermute | solution.py:261
  82.6 7.3 %collective-permute-start.33 = (bf16[2,9,32,128]{3,2,1,0:T(8,128)(2,1)S(1)}, bf16[2,9,32,128]{3,2,1,0:T(8,128)(2,1)S(1)}, u32[]{:S(2)}, u32[]{:S(2)}) collective-permute-start(bf16[2,9,32,128]{3,2,1,0:T(8,128)(2,1)S(1)} %collective-permute-done.30.refs_1_), channel_id=1, source_target_pairs={{0,4},{1,9},{2,6},{3,11},{4,0},{5,13},{6,2},{7,15},{8,12},{9,1},{1... | collective-permute-start | bytes 442376 | tf_op jit(solution)/shard_map/ppermute | solution.py:261
  83.8 5.6 %collective-permute-start.37 = (bf16[1,32,256]{2,1,0:T(8,128)(2,1)S(1)}, bf16[1,32,256]{2,1,0:T(8,128)(2,1)S(1)}, u32[]{:S(2)}, u32[]{:S(2)}) collective-permute-start(bf16[1,32,256]{2,1,0:T(8,128)(2,1)S(1)} %get-tuple-element.174), channel_id=1, source_target_pairs={{1,3},{3,5},{5,7},{7,9},{9,11},{11,13},{13,15},{15,17},{17,19},{19... | collective-permute-start | bytes 49160 | tf_op jit(solution)/shard_map/ppermute | solution.py:399
  85.1 6.6 %collective-permute-start.35 = (bf16[2,9,32,128]{3,2,1,0:T(8,128)(2,1)S(1)}, bf16[2,9,32,128]{3,2,1,0:T(8,128)(2,1)S(1)}, u32[]{:S(2)}, u32[]{:S(2)}) collective-permute-start(bf16[2,9,32,128]{3,2,1,0:T(8,128)(2,1)S(1)} %collective-permute-done.31.refs_2_), channel_id=1, source_target_pairs={{0,8},{1,3},{2,10},{3,1},{4,12},{5,7},{6,14},{7,5},{8,0},{9,11},{1... | collective-permute-start | bytes 442376 | tf_op jit(solution)/shard_map/ppermute | solution.py:261
  88.5 5.1 %collective-permute-start.34 = (bf16[2,9,32,128]{3,2,1,0:T(8,128)(2,1)S(1)}, bf16[2,9,32,128]{3,2,1,0:T(8,128)(2,1)S(1)}, u32[]{:S(2)}, u32[]{:S(2)}) collective-permute-start(bf16[2,9,32,128]{3,2,1,0:T(8,128)(2,1)S(1)} %collective-permute-done.32.refs_4_), channel_id=1, source_target_pairs={{0,2},{1,5},{2,0},{3,7},{4,6},{5,1},{6,4},{7,3},{8,10},{9,13},{10,... | collective-permute-start | bytes 442376 | tf_op jit(solution)/shard_map/ppermute | solution.py:261
  89.4 4.2 %collective-permute-start.38 = (bf16[2,9,32,128]{3,2,1,0:T(8,128)(2,1)S(1)}, bf16[2,9,32,128]{3,2,1,0:T(8,128)(2,1)S(1)}, u32[]{:S(2)}, u32[]{:S(2)}) collective-permute-start(bf16[2,9,32,128]{3,2,1,0:T(8,128)(2,1)S(1)} %shard_map.106.refs_0_), channel_id=1, source_target_pairs={{0,1},{1,0},{2,3},{3,2},{4,5},{5,4},{6,7},{7,6},{8,9},{9,8},{10,11... | collective-permute-start | bytes 442376 | tf_op jit(solution)/shard_map/ppermute | solution.py:266
  89.4 4.7 %collective-permute-start.39 = (bf16[2,9,32,128]{3,2,1,0:T(8,128)(2,1)S(1)}, bf16[2,9,32,128]{3,2,1,0:T(8,128)(2,1)S(1)}, u32[]{:S(2)}, u32[]{:S(2)}) collective-permute-start(bf16[2,9,32,128]{3,2,1,0:T(8,128)(2,1)S(1)} %collective-permute-done.30.refs_1_), channel_id=1, source_target_pairs={{0,1},{1,0},{2,3},{3,2},{4,5},{5,4},{6,7},{7,6},{8,9},{9,8},{10,11... | collective-permute-start | bytes 442376 | tf_op jit(solution)/shard_map/ppermute | solution.py:266
  90.0 4.2 %collective-permute-start.40 = (bf16[2,9,32,128]{3,2,1,0:T(8,128)(2,1)S(1)}, bf16[2,9,32,128]{3,2,1,0:T(8,128)(2,1)S(1)}, u32[]{:S(2)}, u32[]{:S(2)}) collective-permute-start(bf16[2,9,32,128]{3,2,1,0:T(8,128)(2,1)S(1)} %collective-permute-done.31.refs_2_), channel_id=1, source_target_pairs={{0,1},{1,0},{2,3},{3,2},{4,5},{5,4},{6,7},{7,6},{8,9},{9,8},{10,11... | collective-permute-start | bytes 442376 | tf_op jit(solution)/shard_map/ppermute | solution.py:266
  91.7 3.0 %collective-permute-start.42 = (bf16[2,9,32,128]{3,2,1,0:T(8,128)(2,1)S(1)}, bf16[2,9,32,128]{3,2,1,0:T(8,128)(2,1)S(1)}, u32[]{:S(2)}, u32[]{:S(2)}) collective-permute-start(bf16[2,9,32,128]{3,2,1,0:T(8,128)(2,1)S(1)} %collective-permute-done.32.refs_4_), channel_id=1, source_target_pairs={{0,1},{1,0},{2,3},{3,2},{4,5},{5,4},{6,7},{7,6},{8,9},{9,8},{10,11... | collective-permute-start | bytes 442376 | tf_op jit(solution)/shard_map/ppermute | solution.py:266
  93.6 1.4 %collective-permute-start.41 = (bf16[2,9,32,128]{3,2,1,0:T(8,128)(2,1)S(1)}, bf16[2,9,32,128]{3,2,1,0:T(8,128)(2,1)S(1)}, u32[]{:S(2)}, u32[]{:S(2)}) collective-permute-start(bf16[2,9,32,128]{3,2,1,0:T(8,128)(2,1)S(1)} %collective-permute-done.33.refs_3_), channel_id=1, source_target_pairs={{0,1},{1,0},{2,3},{3,2},{4,5},{5,4},{6,7},{7,6},{8,9},{9,8},{10,11... | collective-permute-start | bytes 442376 | tf_op jit(solution)/shard_map/ppermute | solution.py:266
  93.6 1.6 %collective-permute-start.43 = (bf16[2,9,32,128]{3,2,1,0:T(8,128)(2,1)S(1)}, bf16[2,9,32,128]{3,2,1,0:T(8,128)(2,1)S(1)}, u32[]{:S(2)}, u32[]{:S(2)}) collective-permute-start(bf16[2,9,32,128]{3,2,1,0:T(8,128)(2,1)S(1)} %collective-permute-done.34.refs_5_), channel_id=1, source_target_pairs={{0,1},{1,0},{2,3},{3,2},{4,5},{5,4},{6,7},{7,6},{8,9},{9,8},{10,11... | collective-permute-start | bytes 442376 | tf_op jit(solution)/shard_map/ppermute | solution.py:266
  94.1 1.4 %collective-permute-start.44 = (bf16[2,9,32,128]{3,2,1,0:T(8,128)(2,1)S(1)}, bf16[2,9,32,128]{3,2,1,0:T(8,128)(2,1)S(1)}, u32[]{:S(2)}, u32[]{:S(2)}) collective-permute-start(bf16[2,9,32,128]{3,2,1,0:T(8,128)(2,1)S(1)} %collective-permute-done.35.refs_6_), channel_id=1, source_target_pairs={{0,1},{1,0},{2,3},{3,2},{4,5},{5,4},{6,7},{7,6},{8,9},{9,8},{10,11... | collective-permute-start | bytes 442376 | tf_op jit(solution)/shard_map/ppermute | solution.py:266
  94.2 1.5 %collective-permute-start.45 = (bf16[2,9,32,128]{3,2,1,0:T(8,128)(2,1)S(1)}, bf16[2,9,32,128]{3,2,1,0:T(8,128)(2,1)S(1)}, u32[]{:S(2)}, u32[]{:S(2)}) collective-permute-start(bf16[2,9,32,128]{3,2,1,0:T(8,128)(2,1)S(1)} %collective-permute-done.36.refs_7_), channel_id=1, source_target_pairs={{0,1},{1,0},{2,3},{3,2},{4,5},{5,4},{6,7},{7,6},{8,9},{9,8},{10,11... | collective-permute-start | bytes 442376 | tf_op jit(solution)/shard_map/ppermute | solution.py:266
  99.3 2.1 %collective-permute-start.46 = (bf16[4,2,9,32,128]{4,3,2,1,0:T(8,128)(2,1)S(1)}, bf16[4,2,9,32,128]{4,3,2,1,0:T(8,128)(2,1)S(1)}, u32[]{:S(2)}, u32[]{:S(2)}) collective-permute-start(bf16[4,2,9,32,128]{4,3,2,1,0:T(8,128)(2,1)S(1)} %get-tuple-element.185), channel_id=1, source_target_pairs={{0,1},{1,0},{2,3},{3,2},{4,5},{5,4},{6,7},{7,6},{8,9},{9,8},{10,11... | collective-permute-start | bytes 1769480 | tf_op jit(solution)/shard_map/ppermute | solution.py:266
  101.5 10.1 %collective-permute-start.51 = (bf16[4,2,9,32,128]{4,3,2,1,0:T(8,128)(2,1)S(1)}, bf16[4,2,9,32,128]{4,3,2,1,0:T(8,128)(2,1)S(1)}, u32[]{:S(2)}, u32[]{:S(2)}) collective-permute-start(bf16[4,2,9,32,128]{4,3,2,1,0:T(8,128)(2,1)S(1)} %get-tuple-element.195), channel_id=1, source_target_pairs={{0,1},{1,0},{2,3},{3,2},{4,5},{5,4},{6,7},{7,6},{8,9},{9,8},{10,11... | collective-permute-start | bytes 1769480 | tf_op jit(solution)/shard_map/ppermute | solution.py:266
  101.9 6.7 %collective-permute-start.47 = (bf16[2,9,32,128]{3,2,1,0:T(8,128)(2,1)S(1)}, bf16[2,9,32,128]{3,2,1,0:T(8,128)(2,1)S(1)}, u32[]{:S(2)}, u32[]{:S(2)}) collective-permute-start(bf16[2,9,32,128]{3,2,1,0:T(8,128)(2,1)S(1)} %get-tuple-element.191), channel_id=1, source_target_pairs={{0,4},{1,9},{2,6},{3,11},{4,0},{5,13},{6,2},{7,15},{8,12},{9,1},{1... | collective-permute-start | bytes 442376 | tf_op jit(solution)/shard_map/ppermute | solution.py:261
  102.7 5.9 %collective-permute-start.48 = (bf16[2,9,32,128]{3,2,1,0:T(8,128)(2,1)S(1)}, bf16[2,9,32,128]{3,2,1,0:T(8,128)(2,1)S(1)}, u32[]{:S(2)}, u32[]{:S(2)}) collective-permute-start(bf16[2,9,32,128]{3,2,1,0:T(8,128)(2,1)S(1)} %get-tuple-element.192), channel_id=1, source_target_pairs={{0,8},{1,3},{2,10},{3,1},{4,12},{5,7},{6,14},{7,5},{8,0},{9,11},{1... | collective-permute-start | bytes 442376 | tf_op jit(solution)/shard_map/ppermute | solution.py:261
  103.7 6.7 %collective-permute-start.49 = (bf16[2,9,32,128]{3,2,1,0:T(8,128)(2,1)S(1)}, bf16[2,9,32,128]{3,2,1,0:T(8,128)(2,1)S(1)}, u32[]{:S(2)}, u32[]{:S(2)}) collective-permute-start(bf16[2,9,32,128]{3,2,1,0:T(8,128)(2,1)S(1)} %get-tuple-element.193), channel_id=1, source_target_pairs={{0,2},{1,5},{2,0},{3,7},{4,6},{5,1},{6,4},{7,3},{8,10},{9,13},{10,... | collective-permute-start | bytes 442376 | tf_op jit(solution)/shard_map/ppermute | solution.py:261
  104.3 7.4 %collective-permute-start.50 = (bf16[2,9,32,128]{3,2,1,0:T(8,128)(2,1)S(1)}, bf16[2,9,32,128]{3,2,1,0:T(8,128)(2,1)S(1)}, u32[]{:S(2)}, u32[]{:S(2)}) collective-permute-start(bf16[2,9,32,128]{3,2,1,0:T(8,128)(2,1)S(1)} %get-tuple-element.194), channel_id=1, source_target_pairs={{0,12},{1,11},{2,14},{3,9},{4,8},{5,15},{6,10},{7,13},{8,4},{9,3},... | collective-permute-start | bytes 442376 | tf_op jit(solution)/shard_map/ppermute | solution.py:261
  111.9 5.5 %collective-permute-start.52 = (bf16[2,9,32,128]{3,2,1,0:T(8,128)(2,1)S(1)}, bf16[2,9,32,128]{3,2,1,0:T(8,128)(2,1)S(1)}, u32[]{:S(2)}, u32[]{:S(2)}) collective-permute-start(bf16[2,9,32,128]{3,2,1,0:T(8,128)(2,1)S(1)} %get-tuple-element.208), channel_id=1, source_target_pairs={{0,2},{1,5},{2,0},{3,7},{4,6},{5,1},{6,4},{7,3},{8,10},{9,13},{10,... | collective-permute-start | bytes 442376 | tf_op jit(solution)/shard_map/ppermute | solution.py:261
  112.9 5.1 %collective-permute-start.53 = (bf16[2,9,32,128]{3,2,1,0:T(8,128)(2,1)S(1)}, bf16[2,9,32,128]{3,2,1,0:T(8,128)(2,1)S(1)}, u32[]{:S(2)}, u32[]{:S(2)}) collective-permute-start(bf16[2,9,32,128]{3,2,1,0:T(8,128)(2,1)S(1)} %get-tuple-element.209), channel_id=1, source_target_pairs={{0,4},{1,9},{2,6},{3,11},{4,0},{5,13},{6,2},{7,15},{8,12},{9,1},{1... | collective-permute-start | bytes 442376 | tf_op jit(solution)/shard_map/ppermute | solution.py:261
  114.1 5.1 %collective-permute-start.54 = (bf16[2,9,32,128]{3,2,1,0:T(8,128)(2,1)S(1)}, bf16[2,9,32,128]{3,2,1,0:T(8,128)(2,1)S(1)}, u32[]{:S(2)}, u32[]{:S(2)}) collective-permute-start(bf16[2,9,32,128]{3,2,1,0:T(8,128)(2,1)S(1)} %get-tuple-element.210), channel_id=1, source_target_pairs={{0,8},{1,3},{2,10},{3,1},{4,12},{5,7},{6,14},{7,5},{8,0},{9,11},{1... | collective-permute-start | bytes 442376 | tf_op jit(solution)/shard_map/ppermute | solution.py:261
  114.5 1.2 collective-permute-start.55
  114.5 1.3 %collective-permute-start.56 = (bf16[1,32,256]{2,1,0:T(8,128)(2,1)S(1)}, bf16[1,32,256]{2,1,0:T(8,128)(2,1)S(1)}, u32[]{:S(2)}, u32[]{:S(2)}) collective-permute-start(bf16[1,32,256]{2,1,0:T(8,128)(2,1)S(1)} %collective-permute-done.37), channel_id=1, source_target_pairs={{0,1},{1,0},{2,3},{3,2},{4,5},{5,4},{6,7},{7,6},{8,9},{9,8},{10,11... | collective-permute-start | bytes 49160 | tf_op jit(solution)/shard_map/ppermute | solution.py:266
  119.4 5.9 %collective-permute-start.57 = (bf16[9,32,128]{2,1,0:T(8,128)(2,1)S(1)}, bf16[9,32,128]{2,1,0:T(8,128)(2,1)S(1)}, u32[]{:S(2)}, u32[]{:S(2)}) collective-permute-start(bf16[9,32,128]{2,1,0:T(8,128)(2,1)S(1)} %get-tuple-element.219), channel_id=1, source_target_pairs={{0,16},{1,17},{2,18},{3,19},{4,20},{5,21},{6,22},{7,23},{8,24},{9,... | collective-permute-start | bytes 221192 | tf_op jit(solution)/shard_map/ppermute | solution.py:257
  (6 other events, 49.1 us)

commit v21 on v19

--- a/solution.py
+++ b/solution.py
@@ -93,11 +93,17 @@
     emit_coeffs(values, basis_ref, transfer_ref, ranks_ref, out_ref, copies[2].wait)
 
 
-def couple_kernel(source_ref, target_ref, coupling_ref, *refs, order, unroll):
+def couple_kernel(source_ref, target_ref, coupling_ref, *refs, order, joined, unroll):
     chips = sum(len(group) for group in order)
-    in_refs, out_refs, (sources, total) = refs[: 2 * chips], refs[2 * chips : -2], refs[-2:]
+    in_refs, out_refs, (sources, total) = refs[: -2 - 2 * len(order)], refs[-2 - 2 * len(order) : -2], refs[-2:]
     blocks, rank_top, _ = coupling_ref.shape
-    far, mains, rhs, _ = in_refs[0].shape
+    far, mains, rhs, _ = in_refs[-1].shape
+    if joined:
+        cores, in_refs = (in_refs[: len(in_refs) // 2], in_refs[len(in_refs) // 2 :]), []
+        for near_pieces, *far_pieces in cores:
+            pieces = {chip: near_pieces.at[place] for place, chip in enumerate(order[1])}
+            pieces |= dict(zip(order[0], far_pieces))
+            in_refs += [pieces[chip] for chip in range(chips)]
     quads = mains // 3
     clusters = mains + quads
 
@@ -230,7 +236,9 @@
     for i, result in enumerate(results):
         out_ref[i] = result
     if next_refs:
-        coeff_ref, inner_ref, outer_ref = next_refs
+        coeff_ref, inner_ref, outer_ref, values_ref = next_refs
+        for i, result in enumerate(results):
+            values_ref[i] = result
         emit_edges(out_ref, inner_ref, outer_ref)
         emit_coeffs(results, basis_ref, transfer_ref, ranks_ref, coeff_ref)
 
@@ -300,20 +308,21 @@
     )(ranks, charges, basis, transfer)
 
     order = ((x | y | z, x | y, y | z, z | x), (0, x, y, z))
-    couple = pl.pallas_call(
-        functools.partial(couple_kernel, order=order, unroll=64),
-        out_shape=[shape((4, far) + tile_shape, BF)] * 4,
-        in_specs=[SMEM, SMEM, VMEM] + [VMEM] * (cores * chips),
-        out_specs=[VMEM] * 4,
-        scratch_shapes=[
-            pltpu.VMEM((devices * clusters, rhs, LANES), BF),
-            pltpu.VMEM((devices * clusters, rhs, LANES), F32),
-        ],
-        compiler_params=params(24 if devices <= 32 else 60),
-        cost_estimate=pl.CostEstimate(
-            flops=2 * blocks * rhs * rank_top * rank_top, bytes_accessed=10 << 20, transcendentals=0
-        ),
-    )
+    def couple(joined, *args):
+        return pl.pallas_call(
+            functools.partial(couple_kernel, order=order, joined=joined, unroll=64),
+            out_shape=[shape((4, far) + tile_shape, BF)] * 4,
+            in_specs=[SMEM, SMEM] + [VMEM] * (len(args) - 2),
+            out_specs=[VMEM] * 4,
+            scratch_shapes=[
+                pltpu.VMEM((devices * clusters, rhs, LANES), BF),
+                pltpu.VMEM((devices * clusters, rhs, LANES), F32),
+            ],
+            compiler_params=params(24 if devices <= 32 else 60),
+            cost_estimate=pl.CostEstimate(
+                flops=2 * blocks * rhs * rank_top * rank_top, bytes_accessed=10 << 20, transcendentals=0
+            ),
+        )(*args)
 
     near = pl.pallas_call(
         near_kernel,
@@ -365,17 +374,22 @@
         compiler_params=params(16),
     )
     far_add = adder(add_kernel, 2, [part_shape] * 4)
-    middle_add = adder(functools.partial(middle_add_kernel, parts=4), 6, [own_shape] + [part_shape] * 3)
-    last_add = adder(
-        functools.partial(last_add_kernel, parts=3), 4, [shape(tile_shape, F32)] + [tile_out] * (far - 1)
-    )
+    join_near = adder(join_kernel, 4, [shape((4,) + part_shape.shape, BF)])
+
+    def middle_add(*args):
+        kernel = functools.partial(middle_add_kernel, parts=len(args) - 2)
+        return adder(kernel, len(args), [own_shape] + [part_shape] * 3)(*args)
+
+    def last_add(*args):
+        kernel = functools.partial(last_add_kernel, parts=len(args) - 1)
+        return adder(kernel, len(args), [shape(tile_shape, F32)] + [tile_out] * (far - 1))(*args)
 
     def finish(with_coeffs):
         return pl.pallas_call(
             functools.partial(field_kernel, away=far - 1),
-            out_shape=[out_shape, tile_out, edge_shape, edge_shape] if with_coeffs else [out_shape],
+            out_shape=[out_shape, tile_out, edge_shape, edge_shape, out_shape] if with_coeffs else [out_shape],
             in_specs=[SMEM] + [VMEM] * (4 + far),
-            out_specs=[VMEM] * 4 if with_coeffs else [VMEM],
+            out_specs=[VMEM] * 5 if with_coeffs else [VMEM],
             compiler_params=params(16),
         )
 
@@ -388,36 +402,46 @@
         got = {0: column, x: swap(column, x), y: swap(column, y), z: swap(column, z)}
         near_sum = near(field_in, near_field)
         got, near_sum = barrier((got, near_sum))
-        corner = swap(column, x | y | z)
-        other = {chip: swap_cores(part) for chip, part in got.items()}
-        got |= {x | y: swap(got[x], y), y | z: swap(got[y], z), z | x: swap(got[z], x)}
-        got, corner, outer = barrier((got, corner, lax.ppermute(outer, "clu", halo_pairs)))
-        got[x | y | z] = corner
-        other |= {chip: swap_cores(got[chip]) for chip in order[0]}
-        totals = couple(
-            source_rows,
-            target_rows,
-            coupling,
-            *[got[chip] for chip in range(chips)],
-            *[other[chip] for chip in range(chips)],
-        )
-        keep_long, keep, send_long, send = totals
+        second_round = {x | y: swap(got[x], y), y | z: swap(got[y], z), z | x: swap(got[z], x)}
+        if with_coeffs:
+            second_round[x | y | z] = swap(got[x], y | z)
+            (near_pieces,) = join_near(*[got[chip] for chip in order[1]])
+            far_pieces, other_near = barrier(([second_round[chip] for chip in order[0]], swap_cores(near_pieces)))
+            other_far = [swap_cores(part) for part in far_pieces]
+            args = (near_pieces, *far_pieces, other_near, *other_far)
+        else:
+            corner = swap(column, x | y | z)
+            other = {chip: swap_cores(part) for chip, part in got.items()}
+            got |= second_round
+            got, corner, outer = barrier((got, corner, lax.ppermute(outer, "clu", halo_pairs)))
+            got[x | y | z] = corner
+            other |= {chip: swap_cores(got[chip]) for chip in order[0]}
+            args = [got[chip] for chip in range(chips)] + [other[chip] for chip in range(chips)]
+        keep_long, keep, send_long, send = couple(with_coeffs, source_rows, target_rows, coupling, *args)
+
         corner, xy, yz, zx = far_add(keep_long, swap_cores(send_long))
         corner, xy, yz, zx, send = barrier((corner, xy, yz, zx, send))
-        to_x, to_y, to_z, corner, swapped = barrier(
-            (swap(xy, y), swap(yz, z), swap(zx, x), swap(corner, y | z), swap_cores(send))
-        )
-        own, to_x, to_y, to_z, inner, outer = barrier(
-            (*middle_add(keep, swapped, to_x, to_y, to_z, corner), inner, outer)
-        )
-        edges = edge(swap_cores(inner), swap_cores(outer), near_field, near_field)
-        own, to_x, to_y, to_z, edges = barrier((own, swap(to_x, x), swap(to_y, y), swap(to_z, z), edges))
-        total, *away = last_add(own, to_x, to_y, to_z)
-        terms = [swap_far(part, s + 1) for s, part in enumerate(away)]
+        arrived = [swap(xy, y), swap(yz, z), swap(zx, x)]
+        if not with_coeffs:
+            arrived.append(swap(corner, y | z))
+        arrived, swapped = barrier((arrived, swap_cores(send)))
+        (own, *sums), inner, outer = barrier((middle_add(keep, swapped, *arrived), inner, outer))
+        if with_coeffs:
+            parts = [swap(part, way) for part, way in zip(sums + [corner], (x, y, z, x | y | z))]
+            own, parts, inner, outer = barrier((own, parts, inner, lax.ppermute(outer, "clu", halo_pairs)))
+            total, *away = last_add(own, *parts)
+            edges = edge(swap_cores(inner), swap_cores(outer), near_field, near_field)
+            terms, edges = barrier(([swap_far(part, s + 1) for s, part in enumerate(away)], edges))
+        else:
+            edges = edge(swap_cores(inner), swap_cores(outer), near_field, near_field)
+            parts = [swap(part, way) for part, way in zip(sums, (x, y, z))]
+            own, parts, edges = barrier((own, parts, edges))
+            total, *away = last_add(own, *parts)
+            terms = [swap_far(part, s + 1) for s, part in enumerate(away)]
         return finish(with_coeffs)(ranks, near_sum, edges, basis, transfer, total, *terms)
 
-    first, *second_args = apply_matrix(charges, first_coeffs, inner, outer, coupling, True)
-    (second,) = apply_matrix(first, *second_args, coupling, False)
+    first, *second_args, values = apply_matrix(charges, first_coeffs, inner, outer, coupling, True)
+    (second,) = apply_matrix(values, *second_args, coupling, False)
     return (first, second)
 
 

time: 127 us -> 125 us (0.984)
  waiting for transfers between devices: 52.6 us -> 49.2 us
  starting transfers between devices: 50.3 us -> 53 us
    ppermute x28, waiting for transfers between devices: 32.6 us -> 25.5 us  [swap(): lax.ppermute(part, 'clu', [(d, d ^ (turned if d % cores else direction) *...]
    ppermute x2, waiting for transfers between devices: 0.54 us -> 4.32 us  [apply_matrix(): lax.ppermute(outer, 'clu', halo_pairs)]
    ppermute x28, starting transfers between devices: 33.6 us -> 37 us  [swap(): lax.ppermute(part, 'clu', [(d, d ^ (turned if d % cores else direction) *...]
    unnamed x27 -> x25, local copies, waits for them, and re-layouts: 6.54 us -> 5.66 us
    ppermute x24 -> x21, starting transfers between devices: 5.73 us -> 4.99 us  [swap_cores(): return lax.ppermute(part, 'clu', [(d, d ^ 1) for d in range(devices)])]
    ppermute x24 -> x21, waiting for transfers between devices: 7.18 us -> 7.59 us  [swap_cores(): return lax.ppermute(part, 'clu', [(d, d ^ 1) for d in range(devices)])]
    pallas_call x6 -> x7, Pallas kernels: 7.76 us -> 7.82 us  [the longest x2 7.22 us: couple(): pl.pallas_call(functools.partial(couple_kernel, order=order, joined=joine...]
  transfers between devices with their start and end apart: 58 -> 55, of which waited for: 40 -> 39; matrix products, arithmetic and copies ran while one was open for 4% -> 4% of each run, Pallas kernels for 2% -> 2%
where the time goes in v21:
time: 125 us
  starting transfers between devices  53 us (42%)
  waiting for transfers between devices  49.2 us (39%)
  Pallas kernels  16.3 us (13%)
  local copies, waits for them, and re-layouts  5.66 us (5%)
    ppermute x28, starting transfers between devices, swap(): lax.ppermute(part, 'clu', [(d, d ^ (turned if d % cores else direction) *...  37 us
    ppermute x28, waiting for transfers between devices, swap(): lax.ppermute(part, 'clu', [(d, d ^ (turned if d % cores else direction) *...  25.5 us
    ppermute x4, waiting for transfers between devices, swap_far(): lax.ppermute(part, 'clu', [(d, (d + shift * cube) % devices) for d in ran...  11.8 us
    ppermute x4, starting transfers between devices, swap_far(): lax.ppermute(part, 'clu', [(d, (d + shift * cube) % devices) for d in ran...  8.48 us
    ppermute x21, waiting for transfers between devices, swap_cores(): return lax.ppermute(part, 'clu', [(d, d ^ 1) for d in range(devices)])  7.59 us
    pallas_call x2, Pallas kernels, couple(): pl.pallas_call(functools.partial(couple_kernel, order=order, joined=joine...  7.22 us
    unnamed x25, local copies, waits for them, and re-layouts  5.66 us
    ppermute x21, starting transfers between devices, swap_cores(): return lax.ppermute(part, 'clu', [(d, d ^ 1) for d in range(devices)])  4.99 us
  transfers between devices with their start and end apart: 55, of which 39 were waited for; matrix products, arithmetic and copies ran while one was open for 4% of the time, Pallas kernels for 2%

profile of v21, /device:TPU:0, one launch (start us, length us, event | category | flops | bytes accessed | tf_op | source)
XLA Modules:
  0.0 125.0 jit_solution(13514321272736595517)
XLA Ops:
  0.6 2.9 %shard_map.95 = (bf16[9,32,128]{2,1,0:T(8,128)(2,1)}, bf16[1,32,256]{2,1,0:T(8,128)(2,1)}, bf16[1,32,256]{2,1,0:T(8,128)(2,1)}) custom-call(s32[12]{0:T(128)} %ranks_ref.5, bf16[8,32,256]{2,1,0:T(8,128)(2,1)} %v_ref.1, bf16[8,96,256]{2,1,0:T(8,128)(2,1)} %basis_ref.3, bf16[8,96,96]{2,1,0:T(8,128)(2,1)} %transfer_ref.3), custom_call_target="tpu_custom_call" | custom-call | tf_op jit(solution)/shard_map/pallas_call | solution.py:297
  3.6 4.1 %collective-permute-start = (bf16[9,32,128]{2,1,0:T(8,128)(2,1)}, bf16[9,32,128]{2,1,0:T(8,128)(2,1)S(1)}, u32[]{:S(2)}, u32[]{:S(2)}) collective-permute-start(bf16[9,32,128]{2,1,0:T(8,128)(2,1)} %get-tuple-element.109.__.refs_0_), channel_id=1, source_target_pairs={{0,16},{1,17},{2,18},{3,19},{4,20},{5,21},{6,22},{7,23},{8,24},{9,... | collective-permute-start | bytes 221192 | tf_op jit(solution)/shard_map/ppermute | solution.py:265
  7.7 4.8 %copy.10._.coupling_ref = bf16[128,96,96]{2,1,0:T(8,128)(2,1)} copy(bf16[128,96,96]{0,2,1:T(8,128)(2,1)} %param.12) | data formatting | bytes 4718592 | tf_op args[4]
  12.5 0.6 shard_map.96._
  13.0 0.8 copy-done.6
  13.9 1.6 %collective-permute-start.3 = (bf16[2,9,32,128]{3,2,1,0:T(8,128)(2,1)S(1)}, bf16[2,9,32,128]{3,2,1,0:T(8,128)(2,1)S(1)}, u32[]{:S(2)}, u32[]{:S(2)}) collective-permute-start(bf16[2,9,32,128]{3,2,1,0:T(8,128)(2,1)S(1)} %shard_map.97.refs_0_), channel_id=1, source_target_pairs={{0,8},{1,3},{2,10},{3,1},{4,12},{5,7},{6,14},{7,5},{8,0},{9,11},{1... | collective-permute-start | bytes 442376 | tf_op jit(solution)/shard_map/ppermute | solution.py:269
  15.5 1.5 %collective-permute-start.2 = (bf16[2,9,32,128]{3,2,1,0:T(8,128)(2,1)S(1)}, bf16[2,9,32,128]{3,2,1,0:T(8,128)(2,1)S(1)}, u32[]{:S(2)}, u32[]{:S(2)}) collective-permute-start(bf16[2,9,32,128]{3,2,1,0:T(8,128)(2,1)S(1)} %shard_map.97.refs_0_), channel_id=1, source_target_pairs={{0,4},{1,9},{2,6},{3,11},{4,0},{5,13},{6,2},{7,15},{8,12},{9,1},{1... | collective-permute-start | bytes 442376 | tf_op jit(solution)/shard_map/ppermute | solution.py:269
  17.0 1.5 %collective-permute-start.1 = (bf16[2,9,32,128]{3,2,1,0:T(8,128)(2,1)S(1)}, bf16[2,9,32,128]{3,2,1,0:T(8,128)(2,1)S(1)}, u32[]{:S(2)}, u32[]{:S(2)}) collective-permute-start(bf16[2,9,32,128]{3,2,1,0:T(8,128)(2,1)S(1)} %shard_map.97.refs_0_), channel_id=1, source_target_pairs={{0,2},{1,5},{2,0},{3,7},{4,6},{5,1},{6,4},{7,3},{8,10},{9,13},{10,... | collective-permute-start | bytes 442376 | tf_op jit(solution)/shard_map/ppermute | solution.py:269
  18.5 0.6 shard_map.98.near_ref
  19.1 1.3 %collective-permute-done.3.refs_3_ = bf16[2,9,32,128]{3,2,1,0:T(8,128)(2,1)S(1)} collective-permute-done((bf16[2,9,32,128]{3,2,1,0:T(8,128)(2,1)S(1)}, bf16[2,9,32,128]{3,2,1,0:T(8,128)(2,1)S(1)}, u32[]{:S(2)}, u32[]{:S(2)}) %collective-permute-start.3) | collective-permute-done | bytes 147488 | tf_op jit(solution)/shard_map/ppermute | solution.py:269
  20.5 1.3 %collective-permute-done.2.refs_2_ = bf16[2,9,32,128]{3,2,1,0:T(8,128)(2,1)S(1)} collective-permute-done((bf16[2,9,32,128]{3,2,1,0:T(8,128)(2,1)S(1)}, bf16[2,9,32,128]{3,2,1,0:T(8,128)(2,1)S(1)}, u32[]{:S(2)}, u32[]{:S(2)}) %collective-permute-start.2) | collective-permute-done | bytes 147488 | tf_op jit(solution)/shard_map/ppermute | solution.py:269
  22.3 0.5 collective-permute-start.6
  22.8 1.5 %collective-permute-start.7 = (bf16[2,9,32,128]{3,2,1,0:T(8,128)(2,1)S(1)}, bf16[2,9,32,128]{3,2,1,0:T(8,128)(2,1)S(1)}, u32[]{:S(2)}, u32[]{:S(2)}) collective-permute-start(bf16[2,9,32,128]{3,2,1,0:T(8,128)(2,1)S(1)} %collective-permute-done.3.refs_3_), channel_id=1, source_target_pairs={{0,2},{1,5},{2,0},{3,7},{4,6},{5,1},{6,4},{7,3},{8,10},{9,13},{10,... | collective-permute-start | bytes 442376 | tf_op jit(solution)/shard_map/ppermute | solution.py:269
  24.8 2.5 %collective-permute-start.4 = (bf16[2,9,32,128]{3,2,1,0:T(8,128)(2,1)S(1)}, bf16[2,9,32,128]{3,2,1,0:T(8,128)(2,1)S(1)}, u32[]{:S(2)}, u32[]{:S(2)}) collective-permute-start(bf16[2,9,32,128]{3,2,1,0:T(8,128)(2,1)S(1)} %collective-permute-done.1.refs_1_), channel_id=1, source_target_pairs={{0,12},{1,11},{2,14},{3,9},{4,8},{5,15},{6,10},{7,13},{8,4},{9,3},... | collective-permute-start | bytes 442376 | tf_op jit(solution)/shard_map/ppermute | solution.py:269
  27.3 0.9 collective-permute-done.6.refs_3_
  28.6 1.6 %collective-permute-done.5.refs_2_ = bf16[2,9,32,128]{3,2,1,0:T(8,128)(2,1)S(1)} collective-permute-done((bf16[2,9,32,128]{3,2,1,0:T(8,128)(2,1)S(1)}, bf16[2,9,32,128]{3,2,1,0:T(8,128)(2,1)S(1)}, u32[]{:S(2)}, u32[]{:S(2)}) %collective-permute-start.5) | collective-permute-done | bytes 147488 | tf_op jit(solution)/shard_map/ppermute | solution.py:269
  30.2 2.3 %collective-permute-done.4.refs_1_ = bf16[2,9,32,128]{3,2,1,0:T(8,128)(2,1)S(1)} collective-permute-done((bf16[2,9,32,128]{3,2,1,0:T(8,128)(2,1)S(1)}, bf16[2,9,32,128]{3,2,1,0:T(8,128)(2,1)S(1)}, u32[]{:S(2)}, u32[]{:S(2)}) %collective-permute-start.4) | collective-permute-done | bytes 147488 | tf_op jit(solution)/shard_map/ppermute | solution.py:269
  34.9 3.6 %shard_map.101 = (bf16[4,2,9,32,128]{4,3,2,1,0:T(8,128)(2,1)S(1)}, bf16[4,2,9,32,128]{4,3,2,1,0:T(8,128)(2,1)S(1)}, bf16[4,2,9,32,128]{4,3,2,1,0:T(8,128)(2,1)S(1)}, bf16[4,2,9,32,128]{4,3,2,1,0:T(8,128)(2,1)S(1)}) custom-call(s32[128]{0:T(128)S(1)} %bitcast.4, s32[128]{0:T(128)S(1)} %bitcast.6, bf16[128,96,96]{2,1,0:T(8,128)(2,1)S(1)} %copy-done.1, ...), custom_call_target="tpu_custom_call" | custom-call | flops 75497472 | bytes 10485760 | tf_op jit(solution)/shard_map/pallas_call | solution.py:312
  38.8 1.8 %collective-permute-done.13.swap_ref = bf16[4,2,9,32,128]{4,3,2,1,0:T(8,128)(2,1)S(1)} collective-permute-done((bf16[4,2,9,32,128]{4,3,2,1,0:T(8,128)(2,1)S(1)}, bf16[4,2,9,32,128]{4,3,2,1,0:T(8,128)(2,1)S(1)}, u32[]{:S(2)}, u32[]{:S(2)}) %collective-permute-start.13) | collective-permute-done | bytes 589856 | tf_op jit(solution)/shard_map/ppermute | solution.py:274
  41.0 1.0 collective-permute-start.14
  42.5 1.5 %collective-permute-start.16 = (bf16[2,9,32,128]{3,2,1,0:T(8,128)(2,1)S(1)}, bf16[2,9,32,128]{3,2,1,0:T(8,128)(2,1)S(1)}, u32[]{:S(2)}, u32[]{:S(2)}) collective-permute-start(bf16[2,9,32,128]{3,2,1,0:T(8,128)(2,1)S(1)} %get-tuple-element.132), channel_id=1, source_target_pairs={{0,2},{1,5},{2,0},{3,7},{4,6},{5,1},{6,4},{7,3},{8,10},{9,13},{10,... | collective-permute-start | bytes 442376 | tf_op jit(solution)/shard_map/ppermute | solution.py:269
  44.0 2.0 %collective-permute-start.21 = (bf16[2,9,32,128]{3,2,1,0:T(8,128)(2,1)S(1)}, bf16[2,9,32,128]{3,2,1,0:T(8,128)(2,1)S(1)}, u32[]{:S(2)}, u32[]{:S(2)}) collective-permute-start(bf16[2,9,32,128]{3,2,1,0:T(8,128)(2,1)S(1)} %get-tuple-element.148), channel_id=1, source_target_pairs={{0,14},{1,15},{2,12},{3,13},{4,10},{5,11},{6,8},{7,9},{8,6},{9,7},... | collective-permute-start | bytes 442376 | tf_op jit(solution)/shard_map/ppermute | solution.py:269
  46.0 1.6 %collective-permute-done.14.refs_0_ = bf16[2,9,32,128]{3,2,1,0:T(8,128)(2,1)S(1)} collective-permute-done((bf16[2,9,32,128]{3,2,1,0:T(8,128)(2,1)S(1)}, bf16[2,9,32,128]{3,2,1,0:T(8,128)(2,1)S(1)}, u32[]{:S(2)}, u32[]{:S(2)}) %collective-permute-start.14) | collective-permute-done | bytes 147488 | tf_op jit(solution)/shard_map/ppermute | solution.py:269
  47.9 1.9 %collective-permute-done.16.refs_2_ = bf16[2,9,32,128]{3,2,1,0:T(8,128)(2,1)S(1)} collective-permute-done((bf16[2,9,32,128]{3,2,1,0:T(8,128)(2,1)S(1)}, bf16[2,9,32,128]{3,2,1,0:T(8,128)(2,1)S(1)}, u32[]{:S(2)}, u32[]{:S(2)}) %collective-permute-start.16) | collective-permute-done | bytes 147488 | tf_op jit(solution)/shard_map/ppermute | solution.py:269
  50.0 2.5 %collective-permute-start.18 = (bf16[2,9,32,128]{3,2,1,0:T(8,128)(2,1)S(1)}, bf16[2,9,32,128]{3,2,1,0:T(8,128)(2,1)S(1)}, u32[]{:S(2)}, u32[]{:S(2)}) collective-permute-start(bf16[2,9,32,128]{3,2,1,0:T(8,128)(2,1)S(1)} %get-tuple-element.145), channel_id=1, source_target_pairs={{0,2},{1,5},{2,0},{3,7},{4,6},{5,1},{6,4},{7,3},{8,10},{9,13},{10,... | collective-permute-start | bytes 442376 | tf_op jit(solution)/shard_map/ppermute | solution.py:269
  52.5 2.0 %collective-permute-start.20 = (bf16[2,9,32,128]{3,2,1,0:T(8,128)(2,1)S(1)}, bf16[2,9,32,128]{3,2,1,0:T(8,128)(2,1)S(1)}, u32[]{:S(2)}, u32[]{:S(2)}) collective-permute-start(bf16[2,9,32,128]{3,2,1,0:T(8,128)(2,1)S(1)} %get-tuple-element.147), channel_id=1, source_target_pairs={{0,8},{1,3},{2,10},{3,1},{4,12},{5,7},{6,14},{7,5},{8,0},{9,11},{1... | collective-permute-start | bytes 442376 | tf_op jit(solution)/shard_map/ppermute | solution.py:269
  54.6 1.3 %collective-permute-start.22 = (bf16[1,32,256]{2,1,0:T(8,128)(2,1)S(1)}, bf16[1,32,256]{2,1,0:T(8,128)(2,1)S(1)}, u32[]{:S(2)}, u32[]{:S(2)}) collective-permute-start(bf16[1,32,256]{2,1,0:T(8,128)(2,1)S(1)} %copy-done.11), channel_id=1, source_target_pairs={{1,3},{3,5},{5,7},{7,9},{9,11},{11,13},{13,15},{15,17},{17,19},{19... | collective-permute-start | bytes 49160 | tf_op jit(solution)/shard_map/ppermute | solution.py:431
  55.9 4.3 %collective-permute-done.22 = bf16[1,32,256]{2,1,0:T(8,128)(2,1)S(1)} collective-permute-done((bf16[1,32,256]{2,1,0:T(8,128)(2,1)S(1)}, bf16[1,32,256]{2,1,0:T(8,128)(2,1)S(1)}, u32[]{:S(2)}, u32[]{:S(2)}) %collective-permute-start.22) | collective-permute-done | bytes 16416 | tf_op jit(solution)/shard_map/ppermute | solution.py:431
  60.3 1.2 collective-permute-start.23
  62.0 0.7 collective-permute-done.24.inner_ref
  63.0 3.4 %collective-permute-done.23.rest_0_ = bf16[9,32,128]{2,1,0:T(8,128)(2,1)S(1)} collective-permute-done((bf16[9,32,128]{2,1,0:T(8,128)(2,1)S(1)}, bf16[9,32,128]{2,1,0:T(8,128)(2,1)S(1)}, u32[]{:S(2)}, u32[]{:S(2)}) %collective-permute-start.23) | collective-permute-done | bytes 73760 | tf_op jit(solution)/shard_map/ppermute | solution.py:265
  66.4 1.6 %shard_map.106 = (bf16[8,32,256]{2,1,0:T(8,128)(2,1)}, bf16[9,32,128]{2,1,0:T(8,128)(2,1)S(1)}, bf16[1,32,256]{2,1,0:T(8,128)(2,1)S(1)}, bf16[1,32,256]{2,1,0:T(8,128)(2,1)S(1)}, bf16[8,32,256]{2,1,0:T(8,128)(2,1)S(1)}) custom-call(s32[12]{0:T(128)S(1)} %copy-done.7, f32[8,32,256]{2,1,0:T(8,128)S(1)} %shard_map.98.near_ref, ...), custom_call_target="tpu_custom_call" | custom-call | tf_op jit(solution)/shard_map/pallas_call | solution.py:441
  68.5 5.1 %collective-permute-done.26.refs_1_ = bf16[9,32,128]{2,1,0:T(8,128)(2,1)S(1)} collective-permute-done((bf16[9,32,128]{2,1,0:T(8,128)(2,1)S(1)}, bf16[9,32,128]{2,1,0:T(8,128)(2,1)S(1)}, u32[]{:S(2)}, u32[]{:S(2)}) %collective-permute-start.26) | collective-permute-done | bytes 73760 | tf_op jit(solution)/shard_map/ppermute | solution.py:265
  73.6 1.4 %collective-permute-start.28 = (bf16[2,9,32,128]{3,2,1,0:T(8,128)(2,1)S(1)}, bf16[2,9,32,128]{3,2,1,0:T(8,128)(2,1)S(1)}, u32[]{:S(2)}, u32[]{:S(2)}) collective-permute-start(bf16[2,9,32,128]{3,2,1,0:T(8,128)(2,1)S(1)} %shard_map.107.refs_0_), channel_id=1, source_target_pairs={{0,4},{1,9},{2,6},{3,11},{4,0},{5,13},{6,2},{7,15},{8,12},{9,1},{1... | collective-permute-start | bytes 442376 | tf_op jit(solution)/shard_map/ppermute | solution.py:269
  75.0 1.9 %collective-permute-start.27 = (bf16[2,9,32,128]{3,2,1,0:T(8,128)(2,1)S(1)}, bf16[2,9,32,128]{3,2,1,0:T(8,128)(2,1)S(1)}, u32[]{:S(2)}, u32[]{:S(2)}) collective-permute-start(bf16[2,9,32,128]{3,2,1,0:T(8,128)(2,1)S(1)} %shard_map.107.refs_0_), channel_id=1, source_target_pairs={{0,2},{1,5},{2,0},{3,7},{4,6},{5,1},{6,4},{7,3},{8,10},{9,13},{10,... | collective-permute-start | bytes 442376 | tf_op jit(solution)/shard_map/ppermute | solution.py:269
  76.9 0.6 shard_map.108.near_ref
  77.5 1.7 %collective-permute-start.33 = (bf16[2,9,32,128]{3,2,1,0:T(8,128)(2,1)S(1)}, bf16[2,9,32,128]{3,2,1,0:T(8,128)(2,1)S(1)}, u32[]{:S(2)}, u32[]{:S(2)}) collective-permute-start(bf16[2,9,32,128]{3,2,1,0:T(8,128)(2,1)S(1)} %shard_map.107.refs_0_), channel_id=1, source_target_pairs={{0,14},{1,15},{2,12},{3,13},{4,10},{5,11},{6,8},{7,9},{8,6},{9,7},... | collective-permute-start | bytes 442376 | tf_op jit(solution)/shard_map/ppermute | solution.py:269
  79.2 0.9 collective-permute-done.29.refs_4_
  80.4 1.1 collective-permute-start.30
  81.5 1.3 %collective-permute-start.34 = (bf16[1,32,256]{2,1,0:T(8,128)(2,1)S(1)}, bf16[1,32,256]{2,1,0:T(8,128)(2,1)S(1)}, u32[]{:S(2)}, u32[]{:S(2)}) collective-permute-start(bf16[1,32,256]{2,1,0:T(8,128)(2,1)S(1)} %get-tuple-element.170), channel_id=1, source_target_pairs={{1,3},{3,5},{5,7},{7,9},{9,11},{11,13},{13,15},{15,17},{17,19},{19... | collective-permute-start | bytes 49160 | tf_op jit(solution)/shard_map/ppermute | solution.py:416
  82.8 4.4 %collective-permute-start.32 = (bf16[2,9,32,128]{3,2,1,0:T(8,128)(2,1)S(1)}, bf16[2,9,32,128]{3,2,1,0:T(8,128)(2,1)S(1)}, u32[]{:S(2)}, u32[]{:S(2)}) collective-permute-start(bf16[2,9,32,128]{3,2,1,0:T(8,128)(2,1)S(1)} %collective-permute-done.28.refs_2_), channel_id=1, source_target_pairs={{0,8},{1,3},{2,10},{3,1},{4,12},{5,7},{6,14},{7,5},{8,0},{9,11},{1... | collective-permute-start | bytes 442376 | tf_op jit(solution)/shard_map/ppermute | solution.py:269
  87.1 0.7 collective-permute-start.31
  88.4 1.9 %collective-permute-done.32.refs_6_ = bf16[2,9,32,128]{3,2,1,0:T(8,128)(2,1)S(1)} collective-permute-done((bf16[2,9,32,128]{3,2,1,0:T(8,128)(2,1)S(1)}, bf16[2,9,32,128]{3,2,1,0:T(8,128)(2,1)S(1)}, u32[]{:S(2)}, u32[]{:S(2)}) %collective-permute-start.32) | collective-permute-done | bytes 147488 | tf_op jit(solution)/shard_map/ppermute | solution.py:269
  90.4 1.9 %collective-permute-done.31.refs_5_ = bf16[2,9,32,128]{3,2,1,0:T(8,128)(2,1)S(1)} collective-permute-done((bf16[2,9,32,128]{3,2,1,0:T(8,128)(2,1)S(1)}, bf16[2,9,32,128]{3,2,1,0:T(8,128)(2,1)S(1)}, u32[]{:S(2)}, u32[]{:S(2)}) %collective-permute-start.31) | collective-permute-done | bytes 147488 | tf_op jit(solution)/shard_map/ppermute | solution.py:269
  92.3 0.5 collective-permute-start.40
  94.4 3.6 %shard_map.109 = (bf16[4,2,9,32,128]{4,3,2,1,0:T(8,128)(2,1)S(1)}, bf16[4,2,9,32,128]{4,3,2,1,0:T(8,128)(2,1)S(1)}, bf16[4,2,9,32,128]{4,3,2,1,0:T(8,128)(2,1)S(1)}, bf16[4,2,9,32,128]{4,3,2,1,0:T(8,128)(2,1)S(1)}) custom-call(s32[128]{0:T(128)S(1)} %bitcast.5, s32[128]{0:T(128)S(1)} %bitcast.7, bf16[128,96,96]{2,1,0:T(8,128)(2,1)S(1)} %copy-done.1, ...), custom_call_target="tpu_custom_call" | custom-call | flops 75497472 | bytes 10485760 | tf_op jit(solution)/shard_map/pallas_call | solution.py:312
  98.4 1.7 %collective-permute-done.43.swap_ref = bf16[4,2,9,32,128]{4,3,2,1,0:T(8,128)(2,1)S(1)} collective-permute-done((bf16[4,2,9,32,128]{4,3,2,1,0:T(8,128)(2,1)S(1)}, bf16[4,2,9,32,128]{4,3,2,1,0:T(8,128)(2,1)S(1)}, u32[]{:S(2)}, u32[]{:S(2)}) %collective-permute-start.43) | collective-permute-done | bytes 589856 | tf_op jit(solution)/shard_map/ppermute | solution.py:274
  100.6 1.2 collective-permute-start.44
  101.8 0.6 collective-permute-start.45
  102.4 0.7 collective-permute-start.46
  103.1 1.7 %collective-permute-start.47 = (bf16[2,9,32,128]{3,2,1,0:T(8,128)(2,1)S(1)}, bf16[2,9,32,128]{3,2,1,0:T(8,128)(2,1)S(1)}, u32[]{:S(2)}, u32[]{:S(2)}) collective-permute-start(bf16[2,9,32,128]{3,2,1,0:T(8,128)(2,1)S(1)} %get-tuple-element.190), channel_id=1, source_target_pairs={{0,12},{1,11},{2,14},{3,9},{4,8},{5,15},{6,10},{7,13},{8,4},{9,3},... | collective-permute-start | bytes 442376 | tf_op jit(solution)/shard_map/ppermute | solution.py:269
  104.7 2.2 %collective-permute-done.44.refs_0_ = bf16[2,9,32,128]{3,2,1,0:T(8,128)(2,1)S(1)} collective-permute-done((bf16[2,9,32,128]{3,2,1,0:T(8,128)(2,1)S(1)}, bf16[2,9,32,128]{3,2,1,0:T(8,128)(2,1)S(1)}, u32[]{:S(2)}, u32[]{:S(2)}) %collective-permute-start.44) | collective-permute-done | bytes 147488 | tf_op jit(solution)/shard_map/ppermute | solution.py:269
  107.0 1.1 collective-permute-done.45.refs_1_
  108.1 0.9 collective-permute-done.46.refs_2_
  109.0 1.3 %collective-permute-done.47.refs_3_ = bf16[2,9,32,128]{3,2,1,0:T(8,128)(2,1)S(1)} collective-permute-done((bf16[2,9,32,128]{3,2,1,0:T(8,128)(2,1)S(1)}, bf16[2,9,32,128]{3,2,1,0:T(8,128)(2,1)S(1)}, u32[]{:S(2)}, u32[]{:S(2)}) %collective-permute-start.47) | collective-permute-done | bytes 147488 | tf_op jit(solution)/shard_map/ppermute | solution.py:269
  110.6 0.7 collective-permute-start.49
  111.3 0.8 collective-permute-start.50
  112.1 1.0 collective-permute-start.51
  113.6 0.7 collective-permute-done.52.inner_ref
  114.6 1.5 %collective-permute-done.49.refs_0_ = bf16[2,9,32,128]{3,2,1,0:T(8,128)(2,1)S(1)} collective-permute-done((bf16[2,9,32,128]{3,2,1,0:T(8,128)(2,1)S(1)}, bf16[2,9,32,128]{3,2,1,0:T(8,128)(2,1)S(1)}, u32[]{:S(2)}, u32[]{:S(2)}) %collective-permute-start.49) | collective-permute-done | bytes 147488 | tf_op jit(solution)/shard_map/ppermute | solution.py:269
  116.4 0.8 collective-permute-done.51.refs_2_
  117.3 2.8 %collective-permute-start.54 = (bf16[9,32,128]{2,1,0:T(8,128)(2,1)S(1)}, bf16[9,32,128]{2,1,0:T(8,128)(2,1)S(1)}, u32[]{:S(2)}, u32[]{:S(2)}) collective-permute-start(bf16[9,32,128]{2,1,0:T(8,128)(2,1)S(1)} %get-tuple-element.215), channel_id=1, source_target_pairs={{0,16},{1,17},{2,18},{3,19},{4,20},{5,21},{6,22},{7,23},{8,24},{9,... | collective-permute-start | bytes 221192 | tf_op jit(solution)/shard_map/ppermute | solution.py:265
  120.1 3.3 %collective-permute-done.54.rest_0_ = bf16[9,32,128]{2,1,0:T(8,128)(2,1)S(1)} collective-permute-done((bf16[9,32,128]{2,1,0:T(8,128)(2,1)S(1)}, bf16[9,32,128]{2,1,0:T(8,128)(2,1)S(1)}, u32[]{:S(2)}, u32[]{:S(2)}) %collective-permute-start.54) | collective-permute-done | bytes 73760 | tf_op jit(solution)/shard_map/ppermute | solution.py:265
  123.4 1.6 %shard_map.114 = bf16[8,32,256]{2,1,0:T(8,128)(2,1)} custom-call(s32[12]{0:T(128)S(1)} %copy-done.7, f32[8,32,256]{2,1,0:T(8,128)S(1)} %shard_map.108.near_ref, f32[2,32,256]{2,1,0:T(8,128)S(1)} %shard_map.112.edge_ref, bf16[8,96,256]{2,1,0:T(8,128)(2,1)S(1)} %copy-done.2, bf16[8,96,96]{2,1,0:T(8,128)(2,1)S(1)} %copy-done.3, ...), custom_call_target="tpu_custom_call" | custom-call | tf_op jit(solution)/shard_map/pallas_call | solution.py:441
  (91 shorter events, 11.8 us)
Async XLA Ops:
  3.5 9.5 %copy-start.5 = (bf16[9,32,128]{2,1,0:T(8,128)(2,1)S(1)}, bf16[9,32,128]{2,1,0:T(8,128)(2,1)}, u32[]{:S(2)}) copy-start(bf16[9,32,128]{2,1,0:T(8,128)(2,1)} %get-tuple-element.109.__.refs_0_) | copy-start | bytes 221188
  3.5 15.0 %copy-start = (bf16[8,3,256,256]{3,2,1,0:T(8,128)(2,1)S(1)}, bf16[8,3,256,256]{3,2,1,0:T(8,128)(2,1)}, u32[]{:S(2)}) copy-start(bf16[8,3,256,256]{3,2,1,0:T(8,128)(2,1)} %last_ref.3) | copy-start | bytes 9437188
  3.6 15.0 %copy-start.4 = (bf16[8,32,256]{2,1,0:T(8,128)(2,1)S(1)}, bf16[8,32,256]{2,1,0:T(8,128)(2,1)}, u32[]{:S(2)}) copy-start(bf16[8,32,256]{2,1,0:T(8,128)(2,1)} %v_ref.1) | copy-start | bytes 393220
  3.6 9.5 %collective-permute-start = (bf16[9,32,128]{2,1,0:T(8,128)(2,1)}, bf16[9,32,128]{2,1,0:T(8,128)(2,1)S(1)}, u32[]{:S(2)}, u32[]{:S(2)}) collective-permute-start(bf16[9,32,128]{2,1,0:T(8,128)(2,1)} %get-tuple-element.109.__.refs_0_), channel_id=1, source_target_pairs={{0,16},{1,17},{2,18},{3,19},{4,20},{5,21},{6,22},{7,23},{8,24},{9,... | collective-permute-start | bytes 221192 | tf_op jit(solution)/shard_map/ppermute | solution.py:265
  13.0 21.9 %copy-start.1 = (bf16[128,96,96]{2,1,0:T(8,128)(2,1)S(1)}, bf16[128,96,96]{2,1,0:T(8,128)(2,1)}, u32[]{:S(2)}) copy-start(bf16[128,96,96]{2,1,0:T(8,128)(2,1)} %copy.10._.coupling_ref) | copy-start | bytes 7077892
  13.9 19.7 %copy-start.8 = (s32[128]{0:T(128)S(1)}, s32[128]{0:T(128)}, u32[]{:S(2)}) copy-start(s32[128]{0:T(128)} %param.14) | copy-start | bytes 1540
  13.9 19.7 %copy-start.9 = (s32[128]{0:T(128)S(1)}, s32[128]{0:T(128)}, u32[]{:S(2)}) copy-start(s32[128]{0:T(128)} %param.15) | copy-start | bytes 1540
  13.9 6.6 %collective-permute-start.3 = (bf16[2,9,32,128]{3,2,1,0:T(8,128)(2,1)S(1)}, bf16[2,9,32,128]{3,2,1,0:T(8,128)(2,1)S(1)}, u32[]{:S(2)}, u32[]{:S(2)}) collective-permute-start(bf16[2,9,32,128]{3,2,1,0:T(8,128)(2,1)S(1)} %shard_map.97.refs_0_), channel_id=1, source_target_pairs={{0,8},{1,3},{2,10},{3,1},{4,12},{5,7},{6,14},{7,5},{8,0},{9,11},{1... | collective-permute-start | bytes 442376 | tf_op jit(solution)/shard_map/ppermute | solution.py:269
  15.5 6.2 %collective-permute-start.2 = (bf16[2,9,32,128]{3,2,1,0:T(8,128)(2,1)S(1)}, bf16[2,9,32,128]{3,2,1,0:T(8,128)(2,1)S(1)}, u32[]{:S(2)}, u32[]{:S(2)}) collective-permute-start(bf16[2,9,32,128]{3,2,1,0:T(8,128)(2,1)S(1)} %shard_map.97.refs_0_), channel_id=1, source_target_pairs={{0,4},{1,9},{2,6},{3,11},{4,0},{5,13},{6,2},{7,15},{8,12},{9,1},{1... | collective-permute-start | bytes 442376 | tf_op jit(solution)/shard_map/ppermute | solution.py:269
  17.0 5.1 %collective-permute-start.1 = (bf16[2,9,32,128]{3,2,1,0:T(8,128)(2,1)S(1)}, bf16[2,9,32,128]{3,2,1,0:T(8,128)(2,1)S(1)}, u32[]{:S(2)}, u32[]{:S(2)}) collective-permute-start(bf16[2,9,32,128]{3,2,1,0:T(8,128)(2,1)S(1)} %shard_map.97.refs_0_), channel_id=1, source_target_pairs={{0,2},{1,5},{2,0},{3,7},{4,6},{5,1},{6,4},{7,3},{8,10},{9,13},{10,... | collective-permute-start | bytes 442376 | tf_op jit(solution)/shard_map/ppermute | solution.py:269
  22.2 10.3 %collective-permute-start.8 = (bf16[4,2,9,32,128]{4,3,2,1,0:T(8,128)(2,1)S(1)}, bf16[4,2,9,32,128]{4,3,2,1,0:T(8,128)(2,1)S(1)}, u32[]{:S(2)}, u32[]{:S(2)}) collective-permute-start(bf16[4,2,9,32,128]{4,3,2,1,0:T(8,128)(2,1)S(1)} %shard_map.100.refs_0_), channel_id=1, source_target_pairs={{0,1},{1,0},{2,3},{3,2},{4,5},{5,4},{6,7},{7,6},{8,9},{9,8},{10,11... | collective-permute-start | bytes 1769480 | tf_op jit(solution)/shard_map/ppermute | solution.py:274
  22.3 5.9 %collective-permute-start.6 = (bf16[2,9,32,128]{3,2,1,0:T(8,128)(2,1)S(1)}, bf16[2,9,32,128]{3,2,1,0:T(8,128)(2,1)S(1)}, u32[]{:S(2)}, u32[]{:S(2)}) collective-permute-start(bf16[2,9,32,128]{3,2,1,0:T(8,128)(2,1)S(1)} %collective-permute-done.2.refs_2_), channel_id=1, source_target_pairs={{0,8},{1,3},{2,10},{3,1},{4,12},{5,7},{6,14},{7,5},{8,0},{9,11},{1... | collective-permute-start | bytes 442376 | tf_op jit(solution)/shard_map/ppermute | solution.py:269
  22.8 5.7 %collective-permute-start.7 = (bf16[2,9,32,128]{3,2,1,0:T(8,128)(2,1)S(1)}, bf16[2,9,32,128]{3,2,1,0:T(8,128)(2,1)S(1)}, u32[]{:S(2)}, u32[]{:S(2)}) collective-permute-start(bf16[2,9,32,128]{3,2,1,0:T(8,128)(2,1)S(1)} %collective-permute-done.3.refs_3_), channel_id=1, source_target_pairs={{0,2},{1,5},{2,0},{3,7},{4,6},{5,1},{6,4},{7,3},{8,10},{9,13},{10,... | collective-permute-start | bytes 442376 | tf_op jit(solution)/shard_map/ppermute | solution.py:269
  24.3 5.9 %collective-permute-start.5 = (bf16[2,9,32,128]{3,2,1,0:T(8,128)(2,1)S(1)}, bf16[2,9,32,128]{3,2,1,0:T(8,128)(2,1)S(1)}, u32[]{:S(2)}, u32[]{:S(2)}) collective-permute-start(bf16[2,9,32,128]{3,2,1,0:T(8,128)(2,1)S(1)} %collective-permute-done.1.refs_1_), channel_id=1, source_target_pairs={{0,4},{1,9},{2,6},{3,11},{4,0},{5,13},{6,2},{7,15},{8,12},{9,1},{1... | collective-permute-start | bytes 442376 | tf_op jit(solution)/shard_map/ppermute | solution.py:269
  24.8 7.7 %collective-permute-start.4 = (bf16[2,9,32,128]{3,2,1,0:T(8,128)(2,1)S(1)}, bf16[2,9,32,128]{3,2,1,0:T(8,128)(2,1)S(1)}, u32[]{:S(2)}, u32[]{:S(2)}) collective-permute-start(bf16[2,9,32,128]{3,2,1,0:T(8,128)(2,1)S(1)} %collective-permute-done.1.refs_1_), channel_id=1, source_target_pairs={{0,12},{1,11},{2,14},{3,9},{4,8},{5,15},{6,10},{7,13},{8,4},{9,3},... | collective-permute-start | bytes 442376 | tf_op jit(solution)/shard_map/ppermute | solution.py:269
  32.5 1.5 %collective-permute-start.9 = (bf16[2,9,32,128]{3,2,1,0:T(8,128)(2,1)S(1)}, bf16[2,9,32,128]{3,2,1,0:T(8,128)(2,1)S(1)}, u32[]{:S(2)}, u32[]{:S(2)}) collective-permute-start(bf16[2,9,32,128]{3,2,1,0:T(8,128)(2,1)S(1)} %collective-permute-done.4.refs_1_), channel_id=1, source_target_pairs={{0,1},{1,0},{2,3},{3,2},{4,5},{5,4},{6,7},{7,6},{8,9},{9,8},{10,11... | collective-permute-start | bytes 442376 | tf_op jit(solution)/shard_map/ppermute | solution.py:274
  33.0 1.4 %collective-permute-start.10 = (bf16[2,9,32,128]{3,2,1,0:T(8,128)(2,1)S(1)}, bf16[2,9,32,128]{3,2,1,0:T(8,128)(2,1)S(1)}, u32[]{:S(2)}, u32[]{:S(2)}) collective-permute-start(bf16[2,9,32,128]{3,2,1,0:T(8,128)(2,1)S(1)} %collective-permute-done.5.refs_2_), channel_id=1, source_target_pairs={{0,1},{1,0},{2,3},{3,2},{4,5},{5,4},{6,7},{7,6},{8,9},{9,8},{10,11... | collective-permute-start | bytes 442376 | tf_op jit(solution)/shard_map/ppermute | solution.py:274
  33.0 1.6 %collective-permute-start.11 = (bf16[2,9,32,128]{3,2,1,0:T(8,128)(2,1)S(1)}, bf16[2,9,32,128]{3,2,1,0:T(8,128)(2,1)S(1)}, u32[]{:S(2)}, u32[]{:S(2)}) collective-permute-start(bf16[2,9,32,128]{3,2,1,0:T(8,128)(2,1)S(1)} %collective-permute-done.6.refs_3_), channel_id=1, source_target_pairs={{0,1},{1,0},{2,3},{3,2},{4,5},{5,4},{6,7},{7,6},{8,9},{9,8},{10,11... | collective-permute-start | bytes 442376 | tf_op jit(solution)/shard_map/ppermute | solution.py:274
  33.5 1.4 %collective-permute-start.12 = (bf16[2,9,32,128]{3,2,1,0:T(8,128)(2,1)S(1)}, bf16[2,9,32,128]{3,2,1,0:T(8,128)(2,1)S(1)}, u32[]{:S(2)}, u32[]{:S(2)}) collective-permute-start(bf16[2,9,32,128]{3,2,1,0:T(8,128)(2,1)S(1)} %collective-permute-done.7.refs_4_), channel_id=1, source_target_pairs={{0,1},{1,0},{2,3},{3,2},{4,5},{5,4},{6,7},{7,6},{8,9},{9,8},{10,11... | collective-permute-start | bytes 442376 | tf_op jit(solution)/shard_map/ppermute | solution.py:274
  34.9 19.7 %copy-start.11 = (bf16[1,32,256]{2,1,0:T(8,128)(2,1)S(1)}, bf16[1,32,256]{2,1,0:T(8,128)(2,1)}, u32[]{:S(2)}) copy-start(bf16[1,32,256]{2,1,0:T(8,128)(2,1)} %get-tuple-element.150) | copy-start | bytes 49156
  38.5 23.0 %copy-start.10 = (bf16[1,32,256]{2,1,0:T(8,128)(2,1)S(1)}, bf16[1,32,256]{2,1,0:T(8,128)(2,1)}, u32[]{:S(2)}) copy-start(bf16[1,32,256]{2,1,0:T(8,128)(2,1)} %get-tuple-element.157) | copy-start | bytes 49156
  38.5 2.1 %collective-permute-start.13 = (bf16[4,2,9,32,128]{4,3,2,1,0:T(8,128)(2,1)S(1)}, bf16[4,2,9,32,128]{4,3,2,1,0:T(8,128)(2,1)S(1)}, u32[]{:S(2)}, u32[]{:S(2)}) collective-permute-start(bf16[4,2,9,32,128]{4,3,2,1,0:T(8,128)(2,1)S(1)} %get-tuple-element.124), channel_id=1, source_target_pairs={{0,1},{1,0},{2,3},{3,2},{4,5},{5,4},{6,7},{7,6},{8,9},{9,8},{10,11... | collective-permute-start | bytes 1769480 | tf_op jit(solution)/shard_map/ppermute | solution.py:274
  40.7 9.1 %collective-permute-start.17 = (bf16[4,2,9,32,128]{4,3,2,1,0:T(8,128)(2,1)S(1)}, bf16[4,2,9,32,128]{4,3,2,1,0:T(8,128)(2,1)S(1)}, u32[]{:S(2)}, u32[]{:S(2)}) collective-permute-start(bf16[4,2,9,32,128]{4,3,2,1,0:T(8,128)(2,1)S(1)} %get-tuple-element.133), channel_id=1, source_target_pairs={{0,1},{1,0},{2,3},{3,2},{4,5},{5,4},{6,7},{7,6},{8,9},{9,8},{10,11... | collective-permute-start | bytes 1769480 | tf_op jit(solution)/shard_map/ppermute | solution.py:274
  41.0 6.6 %collective-permute-start.14 = (bf16[2,9,32,128]{3,2,1,0:T(8,128)(2,1)S(1)}, bf16[2,9,32,128]{3,2,1,0:T(8,128)(2,1)S(1)}, u32[]{:S(2)}, u32[]{:S(2)}) collective-permute-start(bf16[2,9,32,128]{3,2,1,0:T(8,128)(2,1)S(1)} %get-tuple-element.130), channel_id=1, source_target_pairs={{0,4},{1,9},{2,6},{3,11},{4,0},{5,13},{6,2},{7,15},{8,12},{9,1},{1... | collective-permute-start | bytes 442376 | tf_op jit(solution)/shard_map/ppermute | solution.py:269
  42.0 5.9 %collective-permute-start.15 = (bf16[2,9,32,128]{3,2,1,0:T(8,128)(2,1)S(1)}, bf16[2,9,32,128]{3,2,1,0:T(8,128)(2,1)S(1)}, u32[]{:S(2)}, u32[]{:S(2)}) collective-permute-start(bf16[2,9,32,128]{3,2,1,0:T(8,128)(2,1)S(1)} %get-tuple-element.131), channel_id=1, source_target_pairs={{0,8},{1,3},{2,10},{3,1},{4,12},{5,7},{6,14},{7,5},{8,0},{9,11},{1... | collective-permute-start | bytes 442376 | tf_op jit(solution)/shard_map/ppermute | solution.py:269
  42.5 7.3 %collective-permute-start.16 = (bf16[2,9,32,128]{3,2,1,0:T(8,128)(2,1)S(1)}, bf16[2,9,32,128]{3,2,1,0:T(8,128)(2,1)S(1)}, u32[]{:S(2)}, u32[]{:S(2)}) collective-permute-start(bf16[2,9,32,128]{3,2,1,0:T(8,128)(2,1)S(1)} %get-tuple-element.132), channel_id=1, source_target_pairs={{0,2},{1,5},{2,0},{3,7},{4,6},{5,1},{6,4},{7,3},{8,10},{9,13},{10,... | collective-permute-start | bytes 442376 | tf_op jit(solution)/shard_map/ppermute | solution.py:269
  44.0 11.9 %collective-permute-start.21 = (bf16[2,9,32,128]{3,2,1,0:T(8,128)(2,1)S(1)}, bf16[2,9,32,128]{3,2,1,0:T(8,128)(2,1)S(1)}, u32[]{:S(2)}, u32[]{:S(2)}) collective-permute-start(bf16[2,9,32,128]{3,2,1,0:T(8,128)(2,1)S(1)} %get-tuple-element.148), channel_id=1, source_target_pairs={{0,14},{1,15},{2,12},{3,13},{4,10},{5,11},{6,8},{7,9},{8,6},{9,7},... | collective-permute-start | bytes 442376 | tf_op jit(solution)/shard_map/ppermute | solution.py:269
  50.0 10.2 %collective-permute-start.18 = (bf16[2,9,32,128]{3,2,1,0:T(8,128)(2,1)S(1)}, bf16[2,9,32,128]{3,2,1,0:T(8,128)(2,1)S(1)}, u32[]{:S(2)}, u32[]{:S(2)}) collective-permute-start(bf16[2,9,32,128]{3,2,1,0:T(8,128)(2,1)S(1)} %get-tuple-element.145), channel_id=1, source_target_pairs={{0,2},{1,5},{2,0},{3,7},{4,6},{5,1},{6,4},{7,3},{8,10},{9,13},{10,... | collective-permute-start | bytes 442376 | tf_op jit(solution)/shard_map/ppermute | solution.py:269
  52.5 7.7 %collective-permute-start.19 = (bf16[2,9,32,128]{3,2,1,0:T(8,128)(2,1)S(1)}, bf16[2,9,32,128]{3,2,1,0:T(8,128)(2,1)S(1)}, u32[]{:S(2)}, u32[]{:S(2)}) collective-permute-start(bf16[2,9,32,128]{3,2,1,0:T(8,128)(2,1)S(1)} %get-tuple-element.146), channel_id=1, source_target_pairs={{0,4},{1,9},{2,6},{3,11},{4,0},{5,13},{6,2},{7,15},{8,12},{9,1},{1... | collective-permute-start | bytes 442376 | tf_op jit(solution)/shard_map/ppermute | solution.py:269
  52.5 7.7 %collective-permute-start.20 = (bf16[2,9,32,128]{3,2,1,0:T(8,128)(2,1)S(1)}, bf16[2,9,32,128]{3,2,1,0:T(8,128)(2,1)S(1)}, u32[]{:S(2)}, u32[]{:S(2)}) collective-permute-start(bf16[2,9,32,128]{3,2,1,0:T(8,128)(2,1)S(1)} %get-tuple-element.147), channel_id=1, source_target_pairs={{0,8},{1,3},{2,10},{3,1},{4,12},{5,7},{6,14},{7,5},{8,0},{9,11},{1... | collective-permute-start | bytes 442376 | tf_op jit(solution)/shard_map/ppermute | solution.py:269
  54.6 5.6 %collective-permute-start.22 = (bf16[1,32,256]{2,1,0:T(8,128)(2,1)S(1)}, bf16[1,32,256]{2,1,0:T(8,128)(2,1)S(1)}, u32[]{:S(2)}, u32[]{:S(2)}) collective-permute-start(bf16[1,32,256]{2,1,0:T(8,128)(2,1)S(1)} %copy-done.11), channel_id=1, source_target_pairs={{1,3},{3,5},{5,7},{7,9},{9,11},{11,13},{13,15},{15,17},{17,19},{19... | collective-permute-start | bytes 49160 | tf_op jit(solution)/shard_map/ppermute | solution.py:431
  60.3 6.1 %copy-start.2 = (bf16[8,96,256]{2,1,0:T(8,128)(2,1)S(1)}, bf16[8,96,256]{2,1,0:T(8,128)(2,1)}, u32[]{:S(2)}) copy-start(bf16[8,96,256]{2,1,0:T(8,128)(2,1)} %basis_ref.3) | copy-start | bytes 1179652
  60.3 6.1 %collective-permute-start.23 = (bf16[9,32,128]{2,1,0:T(8,128)(2,1)S(1)}, bf16[9,32,128]{2,1,0:T(8,128)(2,1)S(1)}, u32[]{:S(2)}, u32[]{:S(2)}) collective-permute-start(bf16[9,32,128]{2,1,0:T(8,128)(2,1)S(1)} %get-tuple-element.156), channel_id=1, source_target_pairs={{0,16},{1,17},{2,18},{3,19},{4,20},{5,21},{6,22},{7,23},{8,24},{9,... | collective-permute-start | bytes 221192 | tf_op jit(solution)/shard_map/ppermute | solution.py:265
  61.5 1.2 collective-permute-start.24
  61.5 1.3 %collective-permute-start.25 = (bf16[1,32,256]{2,1,0:T(8,128)(2,1)S(1)}, bf16[1,32,256]{2,1,0:T(8,128)(2,1)S(1)}, u32[]{:S(2)}, u32[]{:S(2)}) collective-permute-start(bf16[1,32,256]{2,1,0:T(8,128)(2,1)S(1)} %collective-permute-done.22), channel_id=1, source_target_pairs={{0,1},{1,0},{2,3},{3,2},{4,5},{5,4},{6,7},{7,6},{8,9},{9,8},{10,11... | collective-permute-start | bytes 49160 | tf_op jit(solution)/shard_map/ppermute | solution.py:274
  68.0 5.5 %collective-permute-start.26 = (bf16[9,32,128]{2,1,0:T(8,128)(2,1)S(1)}, bf16[9,32,128]{2,1,0:T(8,128)(2,1)S(1)}, u32[]{:S(2)}, u32[]{:S(2)}) collective-permute-start(bf16[9,32,128]{2,1,0:T(8,128)(2,1)S(1)} %get-tuple-element.163.refs_0_), channel_id=1, source_target_pairs={{0,16},{1,17},{2,18},{3,19},{4,20},{5,21},{6,22},{7,23},{8,24},{9,... | collective-permute-start | bytes 221192 | tf_op jit(solution)/shard_map/ppermute | solution.py:265
  73.5 6.5 %collective-permute-start.29 = (bf16[2,9,32,128]{3,2,1,0:T(8,128)(2,1)S(1)}, bf16[2,9,32,128]{3,2,1,0:T(8,128)(2,1)S(1)}, u32[]{:S(2)}, u32[]{:S(2)}) collective-permute-start(bf16[2,9,32,128]{3,2,1,0:T(8,128)(2,1)S(1)} %shard_map.107.refs_0_), channel_id=1, source_target_pairs={{0,8},{1,3},{2,10},{3,1},{4,12},{5,7},{6,14},{7,5},{8,0},{9,11},{1... | collective-permute-start | bytes 442376 | tf_op jit(solution)/shard_map/ppermute | solution.py:269
  73.6 6.8 %collective-permute-start.28 = (bf16[2,9,32,128]{3,2,1,0:T(8,128)(2,1)S(1)}, bf16[2,9,32,128]{3,2,1,0:T(8,128)(2,1)S(1)}, u32[]{:S(2)}, u32[]{:S(2)}) collective-permute-start(bf16[2,9,32,128]{3,2,1,0:T(8,128)(2,1)S(1)} %shard_map.107.refs_0_), channel_id=1, source_target_pairs={{0,4},{1,9},{2,6},{3,11},{4,0},{5,13},{6,2},{7,15},{8,12},{9,1},{1... | collective-permute-start | bytes 442376 | tf_op jit(solution)/shard_map/ppermute | solution.py:269
  75.0 5.4 %collective-permute-start.27 = (bf16[2,9,32,128]{3,2,1,0:T(8,128)(2,1)S(1)}, bf16[2,9,32,128]{3,2,1,0:T(8,128)(2,1)S(1)}, u32[]{:S(2)}, u32[]{:S(2)}) collective-permute-start(bf16[2,9,32,128]{3,2,1,0:T(8,128)(2,1)S(1)} %shard_map.107.refs_0_), channel_id=1, source_target_pairs={{0,2},{1,5},{2,0},{3,7},{4,6},{5,1},{6,4},{7,3},{8,10},{9,13},{10,... | collective-permute-start | bytes 442376 | tf_op jit(solution)/shard_map/ppermute | solution.py:269
  77.5 10.3 %collective-permute-start.33 = (bf16[2,9,32,128]{3,2,1,0:T(8,128)(2,1)S(1)}, bf16[2,9,32,128]{3,2,1,0:T(8,128)(2,1)S(1)}, u32[]{:S(2)}, u32[]{:S(2)}) collective-permute-start(bf16[2,9,32,128]{3,2,1,0:T(8,128)(2,1)S(1)} %shard_map.107.refs_0_), channel_id=1, source_target_pairs={{0,14},{1,15},{2,12},{3,13},{4,10},{5,11},{6,8},{7,9},{8,6},{9,7},... | collective-permute-start | bytes 442376 | tf_op jit(solution)/shard_map/ppermute | solution.py:269
  80.4 7.9 %collective-permute-start.30 = (bf16[2,9,32,128]{3,2,1,0:T(8,128)(2,1)S(1)}, bf16[2,9,32,128]{3,2,1,0:T(8,128)(2,1)S(1)}, u32[]{:S(2)}, u32[]{:S(2)}) collective-permute-start(bf16[2,9,32,128]{3,2,1,0:T(8,128)(2,1)S(1)} %collective-permute-done.27.refs_1_), channel_id=1, source_target_pairs={{0,4},{1,9},{2,6},{3,11},{4,0},{5,13},{6,2},{7,15},{8,12},{9,1},{1... | collective-permute-start | bytes 442376 | tf_op jit(solution)/shard_map/ppermute | solution.py:269
  81.5 6.3 %collective-permute-start.34 = (bf16[1,32,256]{2,1,0:T(8,128)(2,1)S(1)}, bf16[1,32,256]{2,1,0:T(8,128)(2,1)S(1)}, u32[]{:S(2)}, u32[]{:S(2)}) collective-permute-start(bf16[1,32,256]{2,1,0:T(8,128)(2,1)S(1)} %get-tuple-element.170), channel_id=1, source_target_pairs={{1,3},{3,5},{5,7},{7,9},{9,11},{11,13},{13,15},{15,17},{17,19},{19... | collective-permute-start | bytes 49160 | tf_op jit(solution)/shard_map/ppermute | solution.py:416
  82.8 7.6 %collective-permute-start.32 = (bf16[2,9,32,128]{3,2,1,0:T(8,128)(2,1)S(1)}, bf16[2,9,32,128]{3,2,1,0:T(8,128)(2,1)S(1)}, u32[]{:S(2)}, u32[]{:S(2)}) collective-permute-start(bf16[2,9,32,128]{3,2,1,0:T(8,128)(2,1)S(1)} %collective-permute-done.28.refs_2_), channel_id=1, source_target_pairs={{0,8},{1,3},{2,10},{3,1},{4,12},{5,7},{6,14},{7,5},{8,0},{9,11},{1... | collective-permute-start | bytes 442376 | tf_op jit(solution)/shard_map/ppermute | solution.py:269
  87.1 5.1 %collective-permute-start.31 = (bf16[2,9,32,128]{3,2,1,0:T(8,128)(2,1)S(1)}, bf16[2,9,32,128]{3,2,1,0:T(8,128)(2,1)S(1)}, u32[]{:S(2)}, u32[]{:S(2)}) collective-permute-start(bf16[2,9,32,128]{3,2,1,0:T(8,128)(2,1)S(1)} %collective-permute-done.29.refs_4_), channel_id=1, source_target_pairs={{0,2},{1,5},{2,0},{3,7},{4,6},{5,1},{6,4},{7,3},{8,10},{9,13},{10,... | collective-permute-start | bytes 442376 | tf_op jit(solution)/shard_map/ppermute | solution.py:269
  87.8 4.5 %collective-permute-start.35 = (bf16[2,9,32,128]{3,2,1,0:T(8,128)(2,1)S(1)}, bf16[2,9,32,128]{3,2,1,0:T(8,128)(2,1)S(1)}, u32[]{:S(2)}, u32[]{:S(2)}) collective-permute-start(bf16[2,9,32,128]{3,2,1,0:T(8,128)(2,1)S(1)} %shard_map.107.refs_0_), channel_id=1, source_target_pairs={{0,1},{1,0},{2,3},{3,2},{4,5},{5,4},{6,7},{7,6},{8,9},{9,8},{10,11... | collective-permute-start | bytes 442376 | tf_op jit(solution)/shard_map/ppermute | solution.py:274
  87.8 5.0 %collective-permute-start.36 = (bf16[2,9,32,128]{3,2,1,0:T(8,128)(2,1)S(1)}, bf16[2,9,32,128]{3,2,1,0:T(8,128)(2,1)S(1)}, u32[]{:S(2)}, u32[]{:S(2)}) collective-permute-start(bf16[2,9,32,128]{3,2,1,0:T(8,128)(2,1)S(1)} %collective-permute-done.27.refs_1_), channel_id=1, source_target_pairs={{0,1},{1,0},{2,3},{3,2},{4,5},{5,4},{6,7},{7,6},{8,9},{9,8},{10,11... | collective-permute-start | bytes 442376 | tf_op jit(solution)/shard_map/ppermute | solution.py:274
  88.3 4.5 %collective-permute-start.37 = (bf16[2,9,32,128]{3,2,1,0:T(8,128)(2,1)S(1)}, bf16[2,9,32,128]{3,2,1,0:T(8,128)(2,1)S(1)}, u32[]{:S(2)}, u32[]{:S(2)}) collective-permute-start(bf16[2,9,32,128]{3,2,1,0:T(8,128)(2,1)S(1)} %collective-permute-done.28.refs_2_), channel_id=1, source_target_pairs={{0,1},{1,0},{2,3},{3,2},{4,5},{5,4},{6,7},{7,6},{8,9},{9,8},{10,11... | collective-permute-start | bytes 442376 | tf_op jit(solution)/shard_map/ppermute | solution.py:274
  90.4 3.0 %collective-permute-start.39 = (bf16[2,9,32,128]{3,2,1,0:T(8,128)(2,1)S(1)}, bf16[2,9,32,128]{3,2,1,0:T(8,128)(2,1)S(1)}, u32[]{:S(2)}, u32[]{:S(2)}) collective-permute-start(bf16[2,9,32,128]{3,2,1,0:T(8,128)(2,1)S(1)} %collective-permute-done.29.refs_4_), channel_id=1, source_target_pairs={{0,1},{1,0},{2,3},{3,2},{4,5},{5,4},{6,7},{7,6},{8,9},{9,8},{10,11... | collective-permute-start | bytes 442376 | tf_op jit(solution)/shard_map/ppermute | solution.py:274
  92.3 1.4 %collective-permute-start.38 = (bf16[2,9,32,128]{3,2,1,0:T(8,128)(2,1)S(1)}, bf16[2,9,32,128]{3,2,1,0:T(8,128)(2,1)S(1)}, u32[]{:S(2)}, u32[]{:S(2)}) collective-permute-start(bf16[2,9,32,128]{3,2,1,0:T(8,128)(2,1)S(1)} %collective-permute-done.30.refs_3_), channel_id=1, source_target_pairs={{0,1},{1,0},{2,3},{3,2},{4,5},{5,4},{6,7},{7,6},{8,9},{9,8},{10,11... | collective-permute-start | bytes 442376 | tf_op jit(solution)/shard_map/ppermute | solution.py:274
  92.3 1.6 %collective-permute-start.40 = (bf16[2,9,32,128]{3,2,1,0:T(8,128)(2,1)S(1)}, bf16[2,9,32,128]{3,2,1,0:T(8,128)(2,1)S(1)}, u32[]{:S(2)}, u32[]{:S(2)}) collective-permute-start(bf16[2,9,32,128]{3,2,1,0:T(8,128)(2,1)S(1)} %collective-permute-done.31.refs_5_), channel_id=1, source_target_pairs={{0,1},{1,0},{2,3},{3,2},{4,5},{5,4},{6,7},{7,6},{8,9},{9,8},{10,11... | collective-permute-start | bytes 442376 | tf_op jit(solution)/shard_map/ppermute | solution.py:274
  92.8 1.4 %collective-permute-start.41 = (bf16[2,9,32,128]{3,2,1,0:T(8,128)(2,1)S(1)}, bf16[2,9,32,128]{3,2,1,0:T(8,128)(2,1)S(1)}, u32[]{:S(2)}, u32[]{:S(2)}) collective-permute-start(bf16[2,9,32,128]{3,2,1,0:T(8,128)(2,1)S(1)} %collective-permute-done.32.refs_6_), channel_id=1, source_target_pairs={{0,1},{1,0},{2,3},{3,2},{4,5},{5,4},{6,7},{7,6},{8,9},{9,8},{10,11... | collective-permute-start | bytes 442376 | tf_op jit(solution)/shard_map/ppermute | solution.py:274
  92.9 1.5 %collective-permute-start.42 = (bf16[2,9,32,128]{3,2,1,0:T(8,128)(2,1)S(1)}, bf16[2,9,32,128]{3,2,1,0:T(8,128)(2,1)S(1)}, u32[]{:S(2)}, u32[]{:S(2)}) collective-permute-start(bf16[2,9,32,128]{3,2,1,0:T(8,128)(2,1)S(1)} %collective-permute-done.33.refs_7_), channel_id=1, source_target_pairs={{0,1},{1,0},{2,3},{3,2},{4,5},{5,4},{6,7},{7,6},{8,9},{9,8},{10,11... | collective-permute-start | bytes 442376 | tf_op jit(solution)/shard_map/ppermute | solution.py:274
  98.0 2.1 %collective-permute-start.43 = (bf16[4,2,9,32,128]{4,3,2,1,0:T(8,128)(2,1)S(1)}, bf16[4,2,9,32,128]{4,3,2,1,0:T(8,128)(2,1)S(1)}, u32[]{:S(2)}, u32[]{:S(2)}) collective-permute-start(bf16[4,2,9,32,128]{4,3,2,1,0:T(8,128)(2,1)S(1)} %get-tuple-element.181), channel_id=1, source_target_pairs={{0,1},{1,0},{2,3},{3,2},{4,5},{5,4},{6,7},{7,6},{8,9},{9,8},{10,11... | collective-permute-start | bytes 1769480 | tf_op jit(solution)/shard_map/ppermute | solution.py:274
  100.2 10.1 %collective-permute-start.48 = (bf16[4,2,9,32,128]{4,3,2,1,0:T(8,128)(2,1)S(1)}, bf16[4,2,9,32,128]{4,3,2,1,0:T(8,128)(2,1)S(1)}, u32[]{:S(2)}, u32[]{:S(2)}) collective-permute-start(bf16[4,2,9,32,128]{4,3,2,1,0:T(8,128)(2,1)S(1)} %get-tuple-element.191), channel_id=1, source_target_pairs={{0,1},{1,0},{2,3},{3,2},{4,5},{5,4},{6,7},{7,6},{8,9},{9,8},{10,11... | collective-permute-start | bytes 1769480 | tf_op jit(solution)/shard_map/ppermute | solution.py:274
  100.6 6.4 %collective-permute-start.44 = (bf16[2,9,32,128]{3,2,1,0:T(8,128)(2,1)S(1)}, bf16[2,9,32,128]{3,2,1,0:T(8,128)(2,1)S(1)}, u32[]{:S(2)}, u32[]{:S(2)}) collective-permute-start(bf16[2,9,32,128]{3,2,1,0:T(8,128)(2,1)S(1)} %get-tuple-element.187), channel_id=1, source_target_pairs={{0,4},{1,9},{2,6},{3,11},{4,0},{5,13},{6,2},{7,15},{8,12},{9,1},{1... | collective-permute-start | bytes 442376 | tf_op jit(solution)/shard_map/ppermute | solution.py:269
  101.8 6.3 %collective-permute-start.45 = (bf16[2,9,32,128]{3,2,1,0:T(8,128)(2,1)S(1)}, bf16[2,9,32,128]{3,2,1,0:T(8,128)(2,1)S(1)}, u32[]{:S(2)}, u32[]{:S(2)}) collective-permute-start(bf16[2,9,32,128]{3,2,1,0:T(8,128)(2,1)S(1)} %get-tuple-element.188), channel_id=1, source_target_pairs={{0,8},{1,3},{2,10},{3,1},{4,12},{5,7},{6,14},{7,5},{8,0},{9,11},{1... | collective-permute-start | bytes 442376 | tf_op jit(solution)/shard_map/ppermute | solution.py:269
  102.4 6.7 %collective-permute-start.46 = (bf16[2,9,32,128]{3,2,1,0:T(8,128)(2,1)S(1)}, bf16[2,9,32,128]{3,2,1,0:T(8,128)(2,1)S(1)}, u32[]{:S(2)}, u32[]{:S(2)}) collective-permute-start(bf16[2,9,32,128]{3,2,1,0:T(8,128)(2,1)S(1)} %get-tuple-element.189), channel_id=1, source_target_pairs={{0,2},{1,5},{2,0},{3,7},{4,6},{5,1},{6,4},{7,3},{8,10},{9,13},{10,... | collective-permute-start | bytes 442376 | tf_op jit(solution)/shard_map/ppermute | solution.py:269
  103.1 7.3 %collective-permute-start.47 = (bf16[2,9,32,128]{3,2,1,0:T(8,128)(2,1)S(1)}, bf16[2,9,32,128]{3,2,1,0:T(8,128)(2,1)S(1)}, u32[]{:S(2)}, u32[]{:S(2)}) collective-permute-start(bf16[2,9,32,128]{3,2,1,0:T(8,128)(2,1)S(1)} %get-tuple-element.190), channel_id=1, source_target_pairs={{0,12},{1,11},{2,14},{3,9},{4,8},{5,15},{6,10},{7,13},{8,4},{9,3},... | collective-permute-start | bytes 442376 | tf_op jit(solution)/shard_map/ppermute | solution.py:269
  110.6 5.5 %collective-permute-start.49 = (bf16[2,9,32,128]{3,2,1,0:T(8,128)(2,1)S(1)}, bf16[2,9,32,128]{3,2,1,0:T(8,128)(2,1)S(1)}, u32[]{:S(2)}, u32[]{:S(2)}) collective-permute-start(bf16[2,9,32,128]{3,2,1,0:T(8,128)(2,1)S(1)} %get-tuple-element.204), channel_id=1, source_target_pairs={{0,2},{1,5},{2,0},{3,7},{4,6},{5,1},{6,4},{7,3},{8,10},{9,13},{10,... | collective-permute-start | bytes 442376 | tf_op jit(solution)/shard_map/ppermute | solution.py:269
  111.3 5.1 %collective-permute-start.50 = (bf16[2,9,32,128]{3,2,1,0:T(8,128)(2,1)S(1)}, bf16[2,9,32,128]{3,2,1,0:T(8,128)(2,1)S(1)}, u32[]{:S(2)}, u32[]{:S(2)}) collective-permute-start(bf16[2,9,32,128]{3,2,1,0:T(8,128)(2,1)S(1)} %get-tuple-element.205), channel_id=1, source_target_pairs={{0,4},{1,9},{2,6},{3,11},{4,0},{5,13},{6,2},{7,15},{8,12},{9,1},{1... | collective-permute-start | bytes 442376 | tf_op jit(solution)/shard_map/ppermute | solution.py:269
  112.1 5.1 %collective-permute-start.51 = (bf16[2,9,32,128]{3,2,1,0:T(8,128)(2,1)S(1)}, bf16[2,9,32,128]{3,2,1,0:T(8,128)(2,1)S(1)}, u32[]{:S(2)}, u32[]{:S(2)}) collective-permute-start(bf16[2,9,32,128]{3,2,1,0:T(8,128)(2,1)S(1)} %get-tuple-element.206), channel_id=1, source_target_pairs={{0,8},{1,3},{2,10},{3,1},{4,12},{5,7},{6,14},{7,5},{8,0},{9,11},{1... | collective-permute-start | bytes 442376 | tf_op jit(solution)/shard_map/ppermute | solution.py:269
  113.1 1.2 collective-permute-start.52
  113.1 1.3 %collective-permute-start.53 = (bf16[1,32,256]{2,1,0:T(8,128)(2,1)S(1)}, bf16[1,32,256]{2,1,0:T(8,128)(2,1)S(1)}, u32[]{:S(2)}, u32[]{:S(2)}) collective-permute-start(bf16[1,32,256]{2,1,0:T(8,128)(2,1)S(1)} %collective-permute-done.34), channel_id=1, source_target_pairs={{0,1},{1,0},{2,3},{3,2},{4,5},{5,4},{6,7},{7,6},{8,9},{9,8},{10,11... | collective-permute-start | bytes 49160 | tf_op jit(solution)/shard_map/ppermute | solution.py:274
  117.3 6.1 %collective-permute-start.54 = (bf16[9,32,128]{2,1,0:T(8,128)(2,1)S(1)}, bf16[9,32,128]{2,1,0:T(8,128)(2,1)S(1)}, u32[]{:S(2)}, u32[]{:S(2)}) collective-permute-start(bf16[9,32,128]{2,1,0:T(8,128)(2,1)S(1)} %get-tuple-element.215), channel_id=1, source_target_pairs={{0,16},{1,17},{2,18},{3,19},{4,20},{5,21},{6,22},{7,23},{8,24},{9,... | collective-permute-start | bytes 221192 | tf_op jit(solution)/shard_map/ppermute | solution.py:265
  (3 other events, 13.1 us)

commit v22 on v21

--- a/solution.py
+++ b/solution.py
@@ -310,7 +310,7 @@
     order = ((x | y | z, x | y, y | z, z | x), (0, x, y, z))
     def couple(joined, *args):
         return pl.pallas_call(
-            functools.partial(couple_kernel, order=order, joined=joined, unroll=64),
+            functools.partial(couple_kernel, order=order, joined=joined, unroll=blocks),
             out_shape=[shape((4, far) + tile_shape, BF)] * 4,
             in_specs=[SMEM, SMEM] + [VMEM] * (len(args) - 2),
             out_specs=[VMEM] * 4,
@@ -426,18 +426,15 @@
             arrived.append(swap(corner, y | z))
         arrived, swapped = barrier((arrived, swap_cores(send)))
         (own, *sums), inner, outer = barrier((middle_add(keep, swapped, *arrived), inner, outer))
+        ways = (x, y, z)
         if with_coeffs:
-            parts = [swap(part, way) for part, way in zip(sums + [corner], (x, y, z, x | y | z))]
-            own, parts, inner, outer = barrier((own, parts, inner, lax.ppermute(outer, "clu", halo_pairs)))
-            total, *away = last_add(own, *parts)
-            edges = edge(swap_cores(inner), swap_cores(outer), near_field, near_field)
-            terms, edges = barrier(([swap_far(part, s + 1) for s, part in enumerate(away)], edges))
-        else:
-            edges = edge(swap_cores(inner), swap_cores(outer), near_field, near_field)
-            parts = [swap(part, way) for part, way in zip(sums, (x, y, z))]
-            own, parts, edges = barrier((own, parts, edges))
-            total, *away = last_add(own, *parts)
-            terms = [swap_far(part, s + 1) for s, part in enumerate(away)]
+            sums, ways = sums + [corner], ways + (x | y | z,)
+            outer = lax.ppermute(outer, "clu", halo_pairs)
+        parts = [swap(part, way) for part, way in zip(sums, ways)]
+        own, parts, inner, outer = barrier((own, parts, inner, outer))
+        total, *away = last_add(own, *parts)
+        edges = edge(swap_cores(inner), swap_cores(outer), near_field, near_field)
+        terms, edges = barrier(([swap_far(part, s + 1) for s, part in enumerate(away)], edges))
         return finish(with_coeffs)(ranks, near_sum, edges, basis, transfer, total, *terms)
 
     first, *second_args, values = apply_matrix(charges, first_coeffs, inner, outer, coupling, True)

time: 125 us -> 125 us (level)
    ppermute x2 -> x1, waiting for transfers between devices: 4.32 us -> 0.01 us  [apply_matrix(): lax.ppermute(outer, 'clu', halo_pairs)]
    ppermute x0 -> x1, waiting for transfers between devices: none -> 4.32 us  [apply_matrix(): outer = lax.ppermute(outer, 'clu', halo_pairs)]
    ppermute x4, waiting for transfers between devices: 11.8 us -> 10.3 us  [swap_far(): lax.ppermute(part, 'clu', [(d, (d + shift * cube) % devices) for d in ran...]
    ppermute x28, waiting for transfers between devices: 25.5 us -> 27 us  [swap(): lax.ppermute(part, 'clu', [(d, d ^ (turned if d % cores else direction) *...]
    ppermute x0 -> x1, starting transfers between devices: none -> 1.28 us  [apply_matrix(): outer = lax.ppermute(outer, 'clu', halo_pairs)]
    ppermute x2 -> x1, starting transfers between devices: 2.56 us -> 1.28 us  [apply_matrix(): lax.ppermute(outer, 'clu', halo_pairs)]
where the time goes in v22:
time: 125 us
  starting transfers between devices  53 us (42%)
  waiting for transfers between devices  49.2 us (39%)
  Pallas kernels  16 us (13%)
  local copies, waits for them, and re-layouts  5.66 us (5%)
    ppermute x28, starting transfers between devices, swap(): lax.ppermute(part, 'clu', [(d, d ^ (turned if d % cores else direction) *...  37 us
    ppermute x28, waiting for transfers between devices, swap(): lax.ppermute(part, 'clu', [(d, d ^ (turned if d % cores else direction) *...  27 us
    ppermute x4, waiting for transfers between devices, swap_far(): lax.ppermute(part, 'clu', [(d, (d + shift * cube) % devices) for d in ran...  10.3 us
    ppermute x4, starting transfers between devices, swap_far(): lax.ppermute(part, 'clu', [(d, (d + shift * cube) % devices) for d in ran...  8.47 us
    ppermute x21, waiting for transfers between devices, swap_cores(): return lax.ppermute(part, 'clu', [(d, d ^ 1) for d in range(devices)])  7.58 us
    pallas_call x2, Pallas kernels, couple(): pl.pallas_call(functools.partial(couple_kernel, order=order, joined=joine...  6.93 us
    unnamed x25, local copies, waits for them, and re-layouts  5.66 us
    ppermute x21, starting transfers between devices, swap_cores(): return lax.ppermute(part, 'clu', [(d, d ^ 1) for d in range(devices)])  5 us
  transfers between devices with their start and end apart: 55, of which 39 were waited for; matrix products, arithmetic and copies ran while one was open for 4% of the time, Pallas kernels for 2%

profile of v22, /device:TPU:0, one launch (start us, length us, event | category | flops | bytes accessed | tf_op | source)
XLA Modules:
  0.0 124.7 jit_solution(1917821190472122791)
XLA Ops:
  0.6 2.9 %shard_map.95 = (bf16[9,32,128]{2,1,0:T(8,128)(2,1)}, bf16[1,32,256]{2,1,0:T(8,128)(2,1)}, bf16[1,32,256]{2,1,0:T(8,128)(2,1)}) custom-call(s32[12]{0:T(128)} %ranks_ref.5, bf16[8,32,256]{2,1,0:T(8,128)(2,1)} %v_ref.1, bf16[8,96,256]{2,1,0:T(8,128)(2,1)} %basis_ref.3, bf16[8,96,96]{2,1,0:T(8,128)(2,1)} %transfer_ref.3), custom_call_target="tpu_custom_call" | custom-call | tf_op jit(solution)/shard_map/pallas_call | solution.py:297
  3.6 4.1 %collective-permute-start = (bf16[9,32,128]{2,1,0:T(8,128)(2,1)}, bf16[9,32,128]{2,1,0:T(8,128)(2,1)S(1)}, u32[]{:S(2)}, u32[]{:S(2)}) collective-permute-start(bf16[9,32,128]{2,1,0:T(8,128)(2,1)} %get-tuple-element.112.__.refs_0_), channel_id=1, source_target_pairs={{0,16},{1,17},{2,18},{3,19},{4,20},{5,21},{6,22},{7,23},{8,24},{9,... | collective-permute-start | bytes 221192 | tf_op jit(solution)/shard_map/ppermute | solution.py:265
  7.7 4.8 %copy.10._.coupling_ref = bf16[128,96,96]{2,1,0:T(8,128)(2,1)} copy(bf16[128,96,96]{0,2,1:T(8,128)(2,1)} %param.12) | data formatting | bytes 4718592 | tf_op args[4]
  12.5 0.6 shard_map.96._
  13.0 0.8 copy-done.6
  13.9 1.6 %collective-permute-start.3 = (bf16[2,9,32,128]{3,2,1,0:T(8,128)(2,1)S(1)}, bf16[2,9,32,128]{3,2,1,0:T(8,128)(2,1)S(1)}, u32[]{:S(2)}, u32[]{:S(2)}) collective-permute-start(bf16[2,9,32,128]{3,2,1,0:T(8,128)(2,1)S(1)} %shard_map.97.refs_0_), channel_id=1, source_target_pairs={{0,8},{1,3},{2,10},{3,1},{4,12},{5,7},{6,14},{7,5},{8,0},{9,11},{1... | collective-permute-start | bytes 442376 | tf_op jit(solution)/shard_map/ppermute | solution.py:269
  15.5 1.5 %collective-permute-start.2 = (bf16[2,9,32,128]{3,2,1,0:T(8,128)(2,1)S(1)}, bf16[2,9,32,128]{3,2,1,0:T(8,128)(2,1)S(1)}, u32[]{:S(2)}, u32[]{:S(2)}) collective-permute-start(bf16[2,9,32,128]{3,2,1,0:T(8,128)(2,1)S(1)} %shard_map.97.refs_0_), channel_id=1, source_target_pairs={{0,4},{1,9},{2,6},{3,11},{4,0},{5,13},{6,2},{7,15},{8,12},{9,1},{1... | collective-permute-start | bytes 442376 | tf_op jit(solution)/shard_map/ppermute | solution.py:269
  17.0 1.5 %collective-permute-start.1 = (bf16[2,9,32,128]{3,2,1,0:T(8,128)(2,1)S(1)}, bf16[2,9,32,128]{3,2,1,0:T(8,128)(2,1)S(1)}, u32[]{:S(2)}, u32[]{:S(2)}) collective-permute-start(bf16[2,9,32,128]{3,2,1,0:T(8,128)(2,1)S(1)} %shard_map.97.refs_0_), channel_id=1, source_target_pairs={{0,2},{1,5},{2,0},{3,7},{4,6},{5,1},{6,4},{7,3},{8,10},{9,13},{10,... | collective-permute-start | bytes 442376 | tf_op jit(solution)/shard_map/ppermute | solution.py:269
  18.5 0.6 shard_map.98.near_ref
  19.1 1.3 %collective-permute-done.3.refs_3_ = bf16[2,9,32,128]{3,2,1,0:T(8,128)(2,1)S(1)} collective-permute-done((bf16[2,9,32,128]{3,2,1,0:T(8,128)(2,1)S(1)}, bf16[2,9,32,128]{3,2,1,0:T(8,128)(2,1)S(1)}, u32[]{:S(2)}, u32[]{:S(2)}) %collective-permute-start.3) | collective-permute-done | bytes 147488 | tf_op jit(solution)/shard_map/ppermute | solution.py:269
  20.5 1.3 %collective-permute-done.2.refs_2_ = bf16[2,9,32,128]{3,2,1,0:T(8,128)(2,1)S(1)} collective-permute-done((bf16[2,9,32,128]{3,2,1,0:T(8,128)(2,1)S(1)}, bf16[2,9,32,128]{3,2,1,0:T(8,128)(2,1)S(1)}, u32[]{:S(2)}, u32[]{:S(2)}) %collective-permute-start.2) | collective-permute-done | bytes 147488 | tf_op jit(solution)/shard_map/ppermute | solution.py:269
  22.3 0.5 collective-permute-start.6
  22.8 1.5 %collective-permute-start.7 = (bf16[2,9,32,128]{3,2,1,0:T(8,128)(2,1)S(1)}, bf16[2,9,32,128]{3,2,1,0:T(8,128)(2,1)S(1)}, u32[]{:S(2)}, u32[]{:S(2)}) collective-permute-start(bf16[2,9,32,128]{3,2,1,0:T(8,128)(2,1)S(1)} %collective-permute-done.3.refs_3_), channel_id=1, source_target_pairs={{0,2},{1,5},{2,0},{3,7},{4,6},{5,1},{6,4},{7,3},{8,10},{9,13},{10,... | collective-permute-start | bytes 442376 | tf_op jit(solution)/shard_map/ppermute | solution.py:269
  24.8 2.5 %collective-permute-start.4 = (bf16[2,9,32,128]{3,2,1,0:T(8,128)(2,1)S(1)}, bf16[2,9,32,128]{3,2,1,0:T(8,128)(2,1)S(1)}, u32[]{:S(2)}, u32[]{:S(2)}) collective-permute-start(bf16[2,9,32,128]{3,2,1,0:T(8,128)(2,1)S(1)} %collective-permute-done.1.refs_1_), channel_id=1, source_target_pairs={{0,12},{1,11},{2,14},{3,9},{4,8},{5,15},{6,10},{7,13},{8,4},{9,3},... | collective-permute-start | bytes 442376 | tf_op jit(solution)/shard_map/ppermute | solution.py:269
  27.3 0.9 collective-permute-done.6.refs_3_
  28.6 1.6 %collective-permute-done.5.refs_2_ = bf16[2,9,32,128]{3,2,1,0:T(8,128)(2,1)S(1)} collective-permute-done((bf16[2,9,32,128]{3,2,1,0:T(8,128)(2,1)S(1)}, bf16[2,9,32,128]{3,2,1,0:T(8,128)(2,1)S(1)}, u32[]{:S(2)}, u32[]{:S(2)}) %collective-permute-start.5) | collective-permute-done | bytes 147488 | tf_op jit(solution)/shard_map/ppermute | solution.py:269
  30.2 2.3 %collective-permute-done.4.refs_1_ = bf16[2,9,32,128]{3,2,1,0:T(8,128)(2,1)S(1)} collective-permute-done((bf16[2,9,32,128]{3,2,1,0:T(8,128)(2,1)S(1)}, bf16[2,9,32,128]{3,2,1,0:T(8,128)(2,1)S(1)}, u32[]{:S(2)}, u32[]{:S(2)}) %collective-permute-start.4) | collective-permute-done | bytes 147488 | tf_op jit(solution)/shard_map/ppermute | solution.py:269
  34.9 3.5 %shard_map.101 = (bf16[4,2,9,32,128]{4,3,2,1,0:T(8,128)(2,1)S(1)}, bf16[4,2,9,32,128]{4,3,2,1,0:T(8,128)(2,1)S(1)}, bf16[4,2,9,32,128]{4,3,2,1,0:T(8,128)(2,1)S(1)}, bf16[4,2,9,32,128]{4,3,2,1,0:T(8,128)(2,1)S(1)}) custom-call(s32[128]{0:T(128)S(1)} %bitcast.4, s32[128]{0:T(128)S(1)} %bitcast.6, bf16[128,96,96]{2,1,0:T(8,128)(2,1)S(1)} %copy-done.1, ...), custom_call_target="tpu_custom_call" | custom-call | flops 75497472 | bytes 10485760 | tf_op jit(solution)/shard_map/pallas_call | solution.py:312
  38.6 1.8 %collective-permute-done.13.swap_ref = bf16[4,2,9,32,128]{4,3,2,1,0:T(8,128)(2,1)S(1)} collective-permute-done((bf16[4,2,9,32,128]{4,3,2,1,0:T(8,128)(2,1)S(1)}, bf16[4,2,9,32,128]{4,3,2,1,0:T(8,128)(2,1)S(1)}, u32[]{:S(2)}, u32[]{:S(2)}) %collective-permute-start.13) | collective-permute-done | bytes 589856 | tf_op jit(solution)/shard_map/ppermute | solution.py:274
  40.9 1.0 collective-permute-start.14
  42.3 1.5 %collective-permute-start.16 = (bf16[2,9,32,128]{3,2,1,0:T(8,128)(2,1)S(1)}, bf16[2,9,32,128]{3,2,1,0:T(8,128)(2,1)S(1)}, u32[]{:S(2)}, u32[]{:S(2)}) collective-permute-start(bf16[2,9,32,128]{3,2,1,0:T(8,128)(2,1)S(1)} %get-tuple-element.135), channel_id=1, source_target_pairs={{0,2},{1,5},{2,0},{3,7},{4,6},{5,1},{6,4},{7,3},{8,10},{9,13},{10,... | collective-permute-start | bytes 442376 | tf_op jit(solution)/shard_map/ppermute | solution.py:269
  43.8 2.0 %collective-permute-start.21 = (bf16[2,9,32,128]{3,2,1,0:T(8,128)(2,1)S(1)}, bf16[2,9,32,128]{3,2,1,0:T(8,128)(2,1)S(1)}, u32[]{:S(2)}, u32[]{:S(2)}) collective-permute-start(bf16[2,9,32,128]{3,2,1,0:T(8,128)(2,1)S(1)} %get-tuple-element.151), channel_id=1, source_target_pairs={{0,14},{1,15},{2,12},{3,13},{4,10},{5,11},{6,8},{7,9},{8,6},{9,7},... | collective-permute-start | bytes 442376 | tf_op jit(solution)/shard_map/ppermute | solution.py:269
  45.8 1.6 %collective-permute-done.14.refs_0_ = bf16[2,9,32,128]{3,2,1,0:T(8,128)(2,1)S(1)} collective-permute-done((bf16[2,9,32,128]{3,2,1,0:T(8,128)(2,1)S(1)}, bf16[2,9,32,128]{3,2,1,0:T(8,128)(2,1)S(1)}, u32[]{:S(2)}, u32[]{:S(2)}) %collective-permute-start.14) | collective-permute-done | bytes 147488 | tf_op jit(solution)/shard_map/ppermute | solution.py:269
  47.8 1.9 %collective-permute-done.16.refs_2_ = bf16[2,9,32,128]{3,2,1,0:T(8,128)(2,1)S(1)} collective-permute-done((bf16[2,9,32,128]{3,2,1,0:T(8,128)(2,1)S(1)}, bf16[2,9,32,128]{3,2,1,0:T(8,128)(2,1)S(1)}, u32[]{:S(2)}, u32[]{:S(2)}) %collective-permute-start.16) | collective-permute-done | bytes 147488 | tf_op jit(solution)/shard_map/ppermute | solution.py:269
  49.9 2.5 %collective-permute-start.18 = (bf16[2,9,32,128]{3,2,1,0:T(8,128)(2,1)S(1)}, bf16[2,9,32,128]{3,2,1,0:T(8,128)(2,1)S(1)}, u32[]{:S(2)}, u32[]{:S(2)}) collective-permute-start(bf16[2,9,32,128]{3,2,1,0:T(8,128)(2,1)S(1)} %get-tuple-element.148), channel_id=1, source_target_pairs={{0,2},{1,5},{2,0},{3,7},{4,6},{5,1},{6,4},{7,3},{8,10},{9,13},{10,... | collective-permute-start | bytes 442376 | tf_op jit(solution)/shard_map/ppermute | solution.py:269
  52.4 2.0 %collective-permute-start.20 = (bf16[2,9,32,128]{3,2,1,0:T(8,128)(2,1)S(1)}, bf16[2,9,32,128]{3,2,1,0:T(8,128)(2,1)S(1)}, u32[]{:S(2)}, u32[]{:S(2)}) collective-permute-start(bf16[2,9,32,128]{3,2,1,0:T(8,128)(2,1)S(1)} %get-tuple-element.150), channel_id=1, source_target_pairs={{0,8},{1,3},{2,10},{3,1},{4,12},{5,7},{6,14},{7,5},{8,0},{9,11},{1... | collective-permute-start | bytes 442376 | tf_op jit(solution)/shard_map/ppermute | solution.py:269
  54.4 1.3 %collective-permute-start.22 = (bf16[1,32,256]{2,1,0:T(8,128)(2,1)S(1)}, bf16[1,32,256]{2,1,0:T(8,128)(2,1)S(1)}, u32[]{:S(2)}, u32[]{:S(2)}) collective-permute-start(bf16[1,32,256]{2,1,0:T(8,128)(2,1)S(1)} %copy-done.11), channel_id=1, source_target_pairs={{1,3},{3,5},{5,7},{7,9},{9,11},{11,13},{13,15},{15,17},{17,19},{19... | collective-permute-start | bytes 49160 | tf_op jit(solution)/shard_map/ppermute | solution.py:432
  55.7 4.3 %collective-permute-done.22 = bf16[1,32,256]{2,1,0:T(8,128)(2,1)S(1)} collective-permute-done((bf16[1,32,256]{2,1,0:T(8,128)(2,1)S(1)}, bf16[1,32,256]{2,1,0:T(8,128)(2,1)S(1)}, u32[]{:S(2)}, u32[]{:S(2)}) %collective-permute-start.22) | collective-permute-done | bytes 16416 | tf_op jit(solution)/shard_map/ppermute | solution.py:432
  60.2 1.2 collective-permute-start.23
  61.9 0.7 collective-permute-done.24.inner_ref
  62.9 3.4 %collective-permute-done.23.rest_0_ = bf16[9,32,128]{2,1,0:T(8,128)(2,1)S(1)} collective-permute-done((bf16[9,32,128]{2,1,0:T(8,128)(2,1)S(1)}, bf16[9,32,128]{2,1,0:T(8,128)(2,1)S(1)}, u32[]{:S(2)}, u32[]{:S(2)}) %collective-permute-start.23) | collective-permute-done | bytes 73760 | tf_op jit(solution)/shard_map/ppermute | solution.py:265
  66.3 1.6 %shard_map.106 = (bf16[8,32,256]{2,1,0:T(8,128)(2,1)}, bf16[9,32,128]{2,1,0:T(8,128)(2,1)S(1)}, bf16[1,32,256]{2,1,0:T(8,128)(2,1)S(1)}, bf16[1,32,256]{2,1,0:T(8,128)(2,1)S(1)}, bf16[8,32,256]{2,1,0:T(8,128)(2,1)S(1)}) custom-call(s32[12]{0:T(128)S(1)} %copy-done.7, f32[8,32,256]{2,1,0:T(8,128)S(1)} %shard_map.98.near_ref, ...), custom_call_target="tpu_custom_call" | custom-call | tf_op jit(solution)/shard_map/pallas_call | solution.py:438
  68.3 5.1 %collective-permute-done.26.refs_1_ = bf16[9,32,128]{2,1,0:T(8,128)(2,1)S(1)} collective-permute-done((bf16[9,32,128]{2,1,0:T(8,128)(2,1)S(1)}, bf16[9,32,128]{2,1,0:T(8,128)(2,1)S(1)}, u32[]{:S(2)}, u32[]{:S(2)}) %collective-permute-start.26) | collective-permute-done | bytes 73760 | tf_op jit(solution)/shard_map/ppermute | solution.py:265
  73.5 1.4 %collective-permute-start.28 = (bf16[2,9,32,128]{3,2,1,0:T(8,128)(2,1)S(1)}, bf16[2,9,32,128]{3,2,1,0:T(8,128)(2,1)S(1)}, u32[]{:S(2)}, u32[]{:S(2)}) collective-permute-start(bf16[2,9,32,128]{3,2,1,0:T(8,128)(2,1)S(1)} %shard_map.107.refs_0_), channel_id=1, source_target_pairs={{0,4},{1,9},{2,6},{3,11},{4,0},{5,13},{6,2},{7,15},{8,12},{9,1},{1... | collective-permute-start | bytes 442376 | tf_op jit(solution)/shard_map/ppermute | solution.py:269
  74.9 1.9 %collective-permute-start.27 = (bf16[2,9,32,128]{3,2,1,0:T(8,128)(2,1)S(1)}, bf16[2,9,32,128]{3,2,1,0:T(8,128)(2,1)S(1)}, u32[]{:S(2)}, u32[]{:S(2)}) collective-permute-start(bf16[2,9,32,128]{3,2,1,0:T(8,128)(2,1)S(1)} %shard_map.107.refs_0_), channel_id=1, source_target_pairs={{0,2},{1,5},{2,0},{3,7},{4,6},{5,1},{6,4},{7,3},{8,10},{9,13},{10,... | collective-permute-start | bytes 442376 | tf_op jit(solution)/shard_map/ppermute | solution.py:269
  76.7 0.6 shard_map.108.near_ref
  77.3 1.7 %collective-permute-start.33 = (bf16[2,9,32,128]{3,2,1,0:T(8,128)(2,1)S(1)}, bf16[2,9,32,128]{3,2,1,0:T(8,128)(2,1)S(1)}, u32[]{:S(2)}, u32[]{:S(2)}) collective-permute-start(bf16[2,9,32,128]{3,2,1,0:T(8,128)(2,1)S(1)} %shard_map.107.refs_0_), channel_id=1, source_target_pairs={{0,14},{1,15},{2,12},{3,13},{4,10},{5,11},{6,8},{7,9},{8,6},{9,7},... | collective-permute-start | bytes 442376 | tf_op jit(solution)/shard_map/ppermute | solution.py:269
  79.0 0.9 collective-permute-done.29.refs_4_
  80.3 1.1 collective-permute-start.30
  81.4 1.3 %collective-permute-start.34 = (bf16[1,32,256]{2,1,0:T(8,128)(2,1)S(1)}, bf16[1,32,256]{2,1,0:T(8,128)(2,1)S(1)}, u32[]{:S(2)}, u32[]{:S(2)}) collective-permute-start(bf16[1,32,256]{2,1,0:T(8,128)(2,1)S(1)} %get-tuple-element.173), channel_id=1, source_target_pairs={{1,3},{3,5},{5,7},{7,9},{9,11},{11,13},{13,15},{15,17},{17,19},{19... | collective-permute-start | bytes 49160 | tf_op jit(solution)/shard_map/ppermute | solution.py:416
  82.6 4.4 %collective-permute-start.32 = (bf16[2,9,32,128]{3,2,1,0:T(8,128)(2,1)S(1)}, bf16[2,9,32,128]{3,2,1,0:T(8,128)(2,1)S(1)}, u32[]{:S(2)}, u32[]{:S(2)}) collective-permute-start(bf16[2,9,32,128]{3,2,1,0:T(8,128)(2,1)S(1)} %collective-permute-done.28.refs_2_), channel_id=1, source_target_pairs={{0,8},{1,3},{2,10},{3,1},{4,12},{5,7},{6,14},{7,5},{8,0},{9,11},{1... | collective-permute-start | bytes 442376 | tf_op jit(solution)/shard_map/ppermute | solution.py:269
  87.0 0.7 collective-permute-start.31
  88.3 1.9 %collective-permute-done.32.refs_6_ = bf16[2,9,32,128]{3,2,1,0:T(8,128)(2,1)S(1)} collective-permute-done((bf16[2,9,32,128]{3,2,1,0:T(8,128)(2,1)S(1)}, bf16[2,9,32,128]{3,2,1,0:T(8,128)(2,1)S(1)}, u32[]{:S(2)}, u32[]{:S(2)}) %collective-permute-start.32) | collective-permute-done | bytes 147488 | tf_op jit(solution)/shard_map/ppermute | solution.py:269
  90.2 1.9 %collective-permute-done.31.refs_5_ = bf16[2,9,32,128]{3,2,1,0:T(8,128)(2,1)S(1)} collective-permute-done((bf16[2,9,32,128]{3,2,1,0:T(8,128)(2,1)S(1)}, bf16[2,9,32,128]{3,2,1,0:T(8,128)(2,1)S(1)}, u32[]{:S(2)}, u32[]{:S(2)}) %collective-permute-start.31) | collective-permute-done | bytes 147488 | tf_op jit(solution)/shard_map/ppermute | solution.py:269
  92.2 0.5 collective-permute-start.40
  94.3 3.5 %shard_map.109 = (bf16[4,2,9,32,128]{4,3,2,1,0:T(8,128)(2,1)S(1)}, bf16[4,2,9,32,128]{4,3,2,1,0:T(8,128)(2,1)S(1)}, bf16[4,2,9,32,128]{4,3,2,1,0:T(8,128)(2,1)S(1)}, bf16[4,2,9,32,128]{4,3,2,1,0:T(8,128)(2,1)S(1)}) custom-call(s32[128]{0:T(128)S(1)} %bitcast.5, s32[128]{0:T(128)S(1)} %bitcast.7, bf16[128,96,96]{2,1,0:T(8,128)(2,1)S(1)} %copy-done.1, ...), custom_call_target="tpu_custom_call" | custom-call | flops 75497472 | bytes 10485760 | tf_op jit(solution)/shard_map/pallas_call | solution.py:312
  98.1 1.7 %collective-permute-done.43.swap_ref = bf16[4,2,9,32,128]{4,3,2,1,0:T(8,128)(2,1)S(1)} collective-permute-done((bf16[4,2,9,32,128]{4,3,2,1,0:T(8,128)(2,1)S(1)}, bf16[4,2,9,32,128]{4,3,2,1,0:T(8,128)(2,1)S(1)}, u32[]{:S(2)}, u32[]{:S(2)}) %collective-permute-start.43) | collective-permute-done | bytes 589856 | tf_op jit(solution)/shard_map/ppermute | solution.py:274
  100.3 1.2 collective-permute-start.44
  101.5 0.6 collective-permute-start.45
  102.1 0.7 collective-permute-start.46
  102.8 1.7 %collective-permute-start.47 = (bf16[2,9,32,128]{3,2,1,0:T(8,128)(2,1)S(1)}, bf16[2,9,32,128]{3,2,1,0:T(8,128)(2,1)S(1)}, u32[]{:S(2)}, u32[]{:S(2)}) collective-permute-start(bf16[2,9,32,128]{3,2,1,0:T(8,128)(2,1)S(1)} %get-tuple-element.193), channel_id=1, source_target_pairs={{0,12},{1,11},{2,14},{3,9},{4,8},{5,15},{6,10},{7,13},{8,4},{9,3},... | collective-permute-start | bytes 442376 | tf_op jit(solution)/shard_map/ppermute | solution.py:269
  104.5 2.2 %collective-permute-done.44.refs_0_ = bf16[2,9,32,128]{3,2,1,0:T(8,128)(2,1)S(1)} collective-permute-done((bf16[2,9,32,128]{3,2,1,0:T(8,128)(2,1)S(1)}, bf16[2,9,32,128]{3,2,1,0:T(8,128)(2,1)S(1)}, u32[]{:S(2)}, u32[]{:S(2)}) %collective-permute-start.44) | collective-permute-done | bytes 147488 | tf_op jit(solution)/shard_map/ppermute | solution.py:269
  106.7 1.1 collective-permute-done.45.refs_1_
  107.8 0.9 collective-permute-done.46.refs_2_
  108.8 1.3 %collective-permute-done.47.refs_3_ = bf16[2,9,32,128]{3,2,1,0:T(8,128)(2,1)S(1)} collective-permute-done((bf16[2,9,32,128]{3,2,1,0:T(8,128)(2,1)S(1)}, bf16[2,9,32,128]{3,2,1,0:T(8,128)(2,1)S(1)}, u32[]{:S(2)}, u32[]{:S(2)}) %collective-permute-start.47) | collective-permute-done | bytes 147488 | tf_op jit(solution)/shard_map/ppermute | solution.py:269
  110.3 0.7 collective-permute-start.49
  111.0 0.8 collective-permute-start.50
  111.8 1.0 collective-permute-start.51
  112.8 3.0 %collective-permute-done.49.refs_0_ = bf16[2,9,32,128]{3,2,1,0:T(8,128)(2,1)S(1)} collective-permute-done((bf16[2,9,32,128]{3,2,1,0:T(8,128)(2,1)S(1)}, bf16[2,9,32,128]{3,2,1,0:T(8,128)(2,1)S(1)}, u32[]{:S(2)}, u32[]{:S(2)}) %collective-permute-start.49) | collective-permute-done | bytes 147488 | tf_op jit(solution)/shard_map/ppermute | solution.py:269
  116.2 0.8 collective-permute-done.51.refs_2_
  117.0 2.8 %collective-permute-start.52 = (bf16[9,32,128]{2,1,0:T(8,128)(2,1)S(1)}, bf16[9,32,128]{2,1,0:T(8,128)(2,1)S(1)}, u32[]{:S(2)}, u32[]{:S(2)}) collective-permute-start(bf16[9,32,128]{2,1,0:T(8,128)(2,1)S(1)} %get-tuple-element.216), channel_id=1, source_target_pairs={{0,16},{1,17},{2,18},{3,19},{4,20},{5,21},{6,22},{7,23},{8,24},{9,... | collective-permute-start | bytes 221192 | tf_op jit(solution)/shard_map/ppermute | solution.py:265
  120.3 0.7 collective-permute-done.53.inner_ref
  121.3 1.8 %collective-permute-done.52.rest_0_ = bf16[9,32,128]{2,1,0:T(8,128)(2,1)S(1)} collective-permute-done((bf16[9,32,128]{2,1,0:T(8,128)(2,1)S(1)}, bf16[9,32,128]{2,1,0:T(8,128)(2,1)S(1)}, u32[]{:S(2)}, u32[]{:S(2)}) %collective-permute-start.52) | collective-permute-done | bytes 73760 | tf_op jit(solution)/shard_map/ppermute | solution.py:265
  123.2 1.6 %shard_map.114 = bf16[8,32,256]{2,1,0:T(8,128)(2,1)} custom-call(s32[12]{0:T(128)S(1)} %copy-done.7, f32[8,32,256]{2,1,0:T(8,128)S(1)} %shard_map.108.near_ref, f32[2,32,256]{2,1,0:T(8,128)S(1)} %shard_map.113.edge_ref, bf16[8,96,256]{2,1,0:T(8,128)(2,1)S(1)} %copy-done.2, bf16[8,96,96]{2,1,0:T(8,128)(2,1)S(1)} %copy-done.3, ...), custom_call_target="tpu_custom_call" | custom-call | tf_op jit(solution)/shard_map/pallas_call | solution.py:438
  (91 shorter events, 11.8 us)
Async XLA Ops:
  3.5 9.5 %copy-start.5 = (bf16[9,32,128]{2,1,0:T(8,128)(2,1)S(1)}, bf16[9,32,128]{2,1,0:T(8,128)(2,1)}, u32[]{:S(2)}) copy-start(bf16[9,32,128]{2,1,0:T(8,128)(2,1)} %get-tuple-element.112.__.refs_0_) | copy-start | bytes 221188
  3.5 15.0 %copy-start = (bf16[8,3,256,256]{3,2,1,0:T(8,128)(2,1)S(1)}, bf16[8,3,256,256]{3,2,1,0:T(8,128)(2,1)}, u32[]{:S(2)}) copy-start(bf16[8,3,256,256]{3,2,1,0:T(8,128)(2,1)} %last_ref.3) | copy-start | bytes 9437188
  3.6 15.0 %copy-start.4 = (bf16[8,32,256]{2,1,0:T(8,128)(2,1)S(1)}, bf16[8,32,256]{2,1,0:T(8,128)(2,1)}, u32[]{:S(2)}) copy-start(bf16[8,32,256]{2,1,0:T(8,128)(2,1)} %v_ref.1) | copy-start | bytes 393220
  3.6 9.5 %collective-permute-start = (bf16[9,32,128]{2,1,0:T(8,128)(2,1)}, bf16[9,32,128]{2,1,0:T(8,128)(2,1)S(1)}, u32[]{:S(2)}, u32[]{:S(2)}) collective-permute-start(bf16[9,32,128]{2,1,0:T(8,128)(2,1)} %get-tuple-element.112.__.refs_0_), channel_id=1, source_target_pairs={{0,16},{1,17},{2,18},{3,19},{4,20},{5,21},{6,22},{7,23},{8,24},{9,... | collective-permute-start | bytes 221192 | tf_op jit(solution)/shard_map/ppermute | solution.py:265
  13.0 21.9 %copy-start.1 = (bf16[128,96,96]{2,1,0:T(8,128)(2,1)S(1)}, bf16[128,96,96]{2,1,0:T(8,128)(2,1)}, u32[]{:S(2)}) copy-start(bf16[128,96,96]{2,1,0:T(8,128)(2,1)} %copy.10._.coupling_ref) | copy-start | bytes 7077892
  13.9 19.7 %copy-start.8 = (s32[128]{0:T(128)S(1)}, s32[128]{0:T(128)}, u32[]{:S(2)}) copy-start(s32[128]{0:T(128)} %param.14) | copy-start | bytes 1540
  13.9 19.7 %copy-start.9 = (s32[128]{0:T(128)S(1)}, s32[128]{0:T(128)}, u32[]{:S(2)}) copy-start(s32[128]{0:T(128)} %param.15) | copy-start | bytes 1540
  13.9 6.6 %collective-permute-start.3 = (bf16[2,9,32,128]{3,2,1,0:T(8,128)(2,1)S(1)}, bf16[2,9,32,128]{3,2,1,0:T(8,128)(2,1)S(1)}, u32[]{:S(2)}, u32[]{:S(2)}) collective-permute-start(bf16[2,9,32,128]{3,2,1,0:T(8,128)(2,1)S(1)} %shard_map.97.refs_0_), channel_id=1, source_target_pairs={{0,8},{1,3},{2,10},{3,1},{4,12},{5,7},{6,14},{7,5},{8,0},{9,11},{1... | collective-permute-start | bytes 442376 | tf_op jit(solution)/shard_map/ppermute | solution.py:269
  15.5 6.2 %collective-permute-start.2 = (bf16[2,9,32,128]{3,2,1,0:T(8,128)(2,1)S(1)}, bf16[2,9,32,128]{3,2,1,0:T(8,128)(2,1)S(1)}, u32[]{:S(2)}, u32[]{:S(2)}) collective-permute-start(bf16[2,9,32,128]{3,2,1,0:T(8,128)(2,1)S(1)} %shard_map.97.refs_0_), channel_id=1, source_target_pairs={{0,4},{1,9},{2,6},{3,11},{4,0},{5,13},{6,2},{7,15},{8,12},{9,1},{1... | collective-permute-start | bytes 442376 | tf_op jit(solution)/shard_map/ppermute | solution.py:269
  17.0 5.1 %collective-permute-start.1 = (bf16[2,9,32,128]{3,2,1,0:T(8,128)(2,1)S(1)}, bf16[2,9,32,128]{3,2,1,0:T(8,128)(2,1)S(1)}, u32[]{:S(2)}, u32[]{:S(2)}) collective-permute-start(bf16[2,9,32,128]{3,2,1,0:T(8,128)(2,1)S(1)} %shard_map.97.refs_0_), channel_id=1, source_target_pairs={{0,2},{1,5},{2,0},{3,7},{4,6},{5,1},{6,4},{7,3},{8,10},{9,13},{10,... | collective-permute-start | bytes 442376 | tf_op jit(solution)/shard_map/ppermute | solution.py:269
  22.2 10.3 %collective-permute-start.8 = (bf16[4,2,9,32,128]{4,3,2,1,0:T(8,128)(2,1)S(1)}, bf16[4,2,9,32,128]{4,3,2,1,0:T(8,128)(2,1)S(1)}, u32[]{:S(2)}, u32[]{:S(2)}) collective-permute-start(bf16[4,2,9,32,128]{4,3,2,1,0:T(8,128)(2,1)S(1)} %shard_map.100.refs_0_), channel_id=1, source_target_pairs={{0,1},{1,0},{2,3},{3,2},{4,5},{5,4},{6,7},{7,6},{8,9},{9,8},{10,11... | collective-permute-start | bytes 1769480 | tf_op jit(solution)/shard_map/ppermute | solution.py:274
  22.3 5.9 %collective-permute-start.6 = (bf16[2,9,32,128]{3,2,1,0:T(8,128)(2,1)S(1)}, bf16[2,9,32,128]{3,2,1,0:T(8,128)(2,1)S(1)}, u32[]{:S(2)}, u32[]{:S(2)}) collective-permute-start(bf16[2,9,32,128]{3,2,1,0:T(8,128)(2,1)S(1)} %collective-permute-done.2.refs_2_), channel_id=1, source_target_pairs={{0,8},{1,3},{2,10},{3,1},{4,12},{5,7},{6,14},{7,5},{8,0},{9,11},{1... | collective-permute-start | bytes 442376 | tf_op jit(solution)/shard_map/ppermute | solution.py:269
  22.8 5.7 %collective-permute-start.7 = (bf16[2,9,32,128]{3,2,1,0:T(8,128)(2,1)S(1)}, bf16[2,9,32,128]{3,2,1,0:T(8,128)(2,1)S(1)}, u32[]{:S(2)}, u32[]{:S(2)}) collective-permute-start(bf16[2,9,32,128]{3,2,1,0:T(8,128)(2,1)S(1)} %collective-permute-done.3.refs_3_), channel_id=1, source_target_pairs={{0,2},{1,5},{2,0},{3,7},{4,6},{5,1},{6,4},{7,3},{8,10},{9,13},{10,... | collective-permute-start | bytes 442376 | tf_op jit(solution)/shard_map/ppermute | solution.py:269
  24.3 5.9 %collective-permute-start.5 = (bf16[2,9,32,128]{3,2,1,0:T(8,128)(2,1)S(1)}, bf16[2,9,32,128]{3,2,1,0:T(8,128)(2,1)S(1)}, u32[]{:S(2)}, u32[]{:S(2)}) collective-permute-start(bf16[2,9,32,128]{3,2,1,0:T(8,128)(2,1)S(1)} %collective-permute-done.1.refs_1_), channel_id=1, source_target_pairs={{0,4},{1,9},{2,6},{3,11},{4,0},{5,13},{6,2},{7,15},{8,12},{9,1},{1... | collective-permute-start | bytes 442376 | tf_op jit(solution)/shard_map/ppermute | solution.py:269
  24.8 7.7 %collective-permute-start.4 = (bf16[2,9,32,128]{3,2,1,0:T(8,128)(2,1)S(1)}, bf16[2,9,32,128]{3,2,1,0:T(8,128)(2,1)S(1)}, u32[]{:S(2)}, u32[]{:S(2)}) collective-permute-start(bf16[2,9,32,128]{3,2,1,0:T(8,128)(2,1)S(1)} %collective-permute-done.1.refs_1_), channel_id=1, source_target_pairs={{0,12},{1,11},{2,14},{3,9},{4,8},{5,15},{6,10},{7,13},{8,4},{9,3},... | collective-permute-start | bytes 442376 | tf_op jit(solution)/shard_map/ppermute | solution.py:269
  32.5 1.5 %collective-permute-start.9 = (bf16[2,9,32,128]{3,2,1,0:T(8,128)(2,1)S(1)}, bf16[2,9,32,128]{3,2,1,0:T(8,128)(2,1)S(1)}, u32[]{:S(2)}, u32[]{:S(2)}) collective-permute-start(bf16[2,9,32,128]{3,2,1,0:T(8,128)(2,1)S(1)} %collective-permute-done.4.refs_1_), channel_id=1, source_target_pairs={{0,1},{1,0},{2,3},{3,2},{4,5},{5,4},{6,7},{7,6},{8,9},{9,8},{10,11... | collective-permute-start | bytes 442376 | tf_op jit(solution)/shard_map/ppermute | solution.py:274
  33.0 1.4 %collective-permute-start.10 = (bf16[2,9,32,128]{3,2,1,0:T(8,128)(2,1)S(1)}, bf16[2,9,32,128]{3,2,1,0:T(8,128)(2,1)S(1)}, u32[]{:S(2)}, u32[]{:S(2)}) collective-permute-start(bf16[2,9,32,128]{3,2,1,0:T(8,128)(2,1)S(1)} %collective-permute-done.5.refs_2_), channel_id=1, source_target_pairs={{0,1},{1,0},{2,3},{3,2},{4,5},{5,4},{6,7},{7,6},{8,9},{9,8},{10,11... | collective-permute-start | bytes 442376 | tf_op jit(solution)/shard_map/ppermute | solution.py:274
  33.0 1.6 %collective-permute-start.11 = (bf16[2,9,32,128]{3,2,1,0:T(8,128)(2,1)S(1)}, bf16[2,9,32,128]{3,2,1,0:T(8,128)(2,1)S(1)}, u32[]{:S(2)}, u32[]{:S(2)}) collective-permute-start(bf16[2,9,32,128]{3,2,1,0:T(8,128)(2,1)S(1)} %collective-permute-done.6.refs_3_), channel_id=1, source_target_pairs={{0,1},{1,0},{2,3},{3,2},{4,5},{5,4},{6,7},{7,6},{8,9},{9,8},{10,11... | collective-permute-start | bytes 442376 | tf_op jit(solution)/shard_map/ppermute | solution.py:274
  33.5 1.4 %collective-permute-start.12 = (bf16[2,9,32,128]{3,2,1,0:T(8,128)(2,1)S(1)}, bf16[2,9,32,128]{3,2,1,0:T(8,128)(2,1)S(1)}, u32[]{:S(2)}, u32[]{:S(2)}) collective-permute-start(bf16[2,9,32,128]{3,2,1,0:T(8,128)(2,1)S(1)} %collective-permute-done.7.refs_4_), channel_id=1, source_target_pairs={{0,1},{1,0},{2,3},{3,2},{4,5},{5,4},{6,7},{7,6},{8,9},{9,8},{10,11... | collective-permute-start | bytes 442376 | tf_op jit(solution)/shard_map/ppermute | solution.py:274
  34.9 19.5 %copy-start.11 = (bf16[1,32,256]{2,1,0:T(8,128)(2,1)S(1)}, bf16[1,32,256]{2,1,0:T(8,128)(2,1)}, u32[]{:S(2)}) copy-start(bf16[1,32,256]{2,1,0:T(8,128)(2,1)} %get-tuple-element.153) | copy-start | bytes 49156
  38.4 23.0 %copy-start.10 = (bf16[1,32,256]{2,1,0:T(8,128)(2,1)S(1)}, bf16[1,32,256]{2,1,0:T(8,128)(2,1)}, u32[]{:S(2)}) copy-start(bf16[1,32,256]{2,1,0:T(8,128)(2,1)} %get-tuple-element.160) | copy-start | bytes 49156
  38.4 2.1 %collective-permute-start.13 = (bf16[4,2,9,32,128]{4,3,2,1,0:T(8,128)(2,1)S(1)}, bf16[4,2,9,32,128]{4,3,2,1,0:T(8,128)(2,1)S(1)}, u32[]{:S(2)}, u32[]{:S(2)}) collective-permute-start(bf16[4,2,9,32,128]{4,3,2,1,0:T(8,128)(2,1)S(1)} %get-tuple-element.127), channel_id=1, source_target_pairs={{0,1},{1,0},{2,3},{3,2},{4,5},{5,4},{6,7},{7,6},{8,9},{9,8},{10,11... | collective-permute-start | bytes 1769480 | tf_op jit(solution)/shard_map/ppermute | solution.py:274
  40.6 9.1 %collective-permute-start.17 = (bf16[4,2,9,32,128]{4,3,2,1,0:T(8,128)(2,1)S(1)}, bf16[4,2,9,32,128]{4,3,2,1,0:T(8,128)(2,1)S(1)}, u32[]{:S(2)}, u32[]{:S(2)}) collective-permute-start(bf16[4,2,9,32,128]{4,3,2,1,0:T(8,128)(2,1)S(1)} %get-tuple-element.136), channel_id=1, source_target_pairs={{0,1},{1,0},{2,3},{3,2},{4,5},{5,4},{6,7},{7,6},{8,9},{9,8},{10,11... | collective-permute-start | bytes 1769480 | tf_op jit(solution)/shard_map/ppermute | solution.py:274
  40.9 6.6 %collective-permute-start.14 = (bf16[2,9,32,128]{3,2,1,0:T(8,128)(2,1)S(1)}, bf16[2,9,32,128]{3,2,1,0:T(8,128)(2,1)S(1)}, u32[]{:S(2)}, u32[]{:S(2)}) collective-permute-start(bf16[2,9,32,128]{3,2,1,0:T(8,128)(2,1)S(1)} %get-tuple-element.133), channel_id=1, source_target_pairs={{0,4},{1,9},{2,6},{3,11},{4,0},{5,13},{6,2},{7,15},{8,12},{9,1},{1... | collective-permute-start | bytes 442376 | tf_op jit(solution)/shard_map/ppermute | solution.py:269
  41.9 5.9 %collective-permute-start.15 = (bf16[2,9,32,128]{3,2,1,0:T(8,128)(2,1)S(1)}, bf16[2,9,32,128]{3,2,1,0:T(8,128)(2,1)S(1)}, u32[]{:S(2)}, u32[]{:S(2)}) collective-permute-start(bf16[2,9,32,128]{3,2,1,0:T(8,128)(2,1)S(1)} %get-tuple-element.134), channel_id=1, source_target_pairs={{0,8},{1,3},{2,10},{3,1},{4,12},{5,7},{6,14},{7,5},{8,0},{9,11},{1... | collective-permute-start | bytes 442376 | tf_op jit(solution)/shard_map/ppermute | solution.py:269
  42.3 7.3 %collective-permute-start.16 = (bf16[2,9,32,128]{3,2,1,0:T(8,128)(2,1)S(1)}, bf16[2,9,32,128]{3,2,1,0:T(8,128)(2,1)S(1)}, u32[]{:S(2)}, u32[]{:S(2)}) collective-permute-start(bf16[2,9,32,128]{3,2,1,0:T(8,128)(2,1)S(1)} %get-tuple-element.135), channel_id=1, source_target_pairs={{0,2},{1,5},{2,0},{3,7},{4,6},{5,1},{6,4},{7,3},{8,10},{9,13},{10,... | collective-permute-start | bytes 442376 | tf_op jit(solution)/shard_map/ppermute | solution.py:269
  43.8 11.9 %collective-permute-start.21 = (bf16[2,9,32,128]{3,2,1,0:T(8,128)(2,1)S(1)}, bf16[2,9,32,128]{3,2,1,0:T(8,128)(2,1)S(1)}, u32[]{:S(2)}, u32[]{:S(2)}) collective-permute-start(bf16[2,9,32,128]{3,2,1,0:T(8,128)(2,1)S(1)} %get-tuple-element.151), channel_id=1, source_target_pairs={{0,14},{1,15},{2,12},{3,13},{4,10},{5,11},{6,8},{7,9},{8,6},{9,7},... | collective-permute-start | bytes 442376 | tf_op jit(solution)/shard_map/ppermute | solution.py:269
  49.9 10.2 %collective-permute-start.18 = (bf16[2,9,32,128]{3,2,1,0:T(8,128)(2,1)S(1)}, bf16[2,9,32,128]{3,2,1,0:T(8,128)(2,1)S(1)}, u32[]{:S(2)}, u32[]{:S(2)}) collective-permute-start(bf16[2,9,32,128]{3,2,1,0:T(8,128)(2,1)S(1)} %get-tuple-element.148), channel_id=1, source_target_pairs={{0,2},{1,5},{2,0},{3,7},{4,6},{5,1},{6,4},{7,3},{8,10},{9,13},{10,... | collective-permute-start | bytes 442376 | tf_op jit(solution)/shard_map/ppermute | solution.py:269
  52.4 7.7 %collective-permute-start.19 = (bf16[2,9,32,128]{3,2,1,0:T(8,128)(2,1)S(1)}, bf16[2,9,32,128]{3,2,1,0:T(8,128)(2,1)S(1)}, u32[]{:S(2)}, u32[]{:S(2)}) collective-permute-start(bf16[2,9,32,128]{3,2,1,0:T(8,128)(2,1)S(1)} %get-tuple-element.149), channel_id=1, source_target_pairs={{0,4},{1,9},{2,6},{3,11},{4,0},{5,13},{6,2},{7,15},{8,12},{9,1},{1... | collective-permute-start | bytes 442376 | tf_op jit(solution)/shard_map/ppermute | solution.py:269
  52.4 7.7 %collective-permute-start.20 = (bf16[2,9,32,128]{3,2,1,0:T(8,128)(2,1)S(1)}, bf16[2,9,32,128]{3,2,1,0:T(8,128)(2,1)S(1)}, u32[]{:S(2)}, u32[]{:S(2)}) collective-permute-start(bf16[2,9,32,128]{3,2,1,0:T(8,128)(2,1)S(1)} %get-tuple-element.150), channel_id=1, source_target_pairs={{0,8},{1,3},{2,10},{3,1},{4,12},{5,7},{6,14},{7,5},{8,0},{9,11},{1... | collective-permute-start | bytes 442376 | tf_op jit(solution)/shard_map/ppermute | solution.py:269
  54.4 5.6 %collective-permute-start.22 = (bf16[1,32,256]{2,1,0:T(8,128)(2,1)S(1)}, bf16[1,32,256]{2,1,0:T(8,128)(2,1)S(1)}, u32[]{:S(2)}, u32[]{:S(2)}) collective-permute-start(bf16[1,32,256]{2,1,0:T(8,128)(2,1)S(1)} %copy-done.11), channel_id=1, source_target_pairs={{1,3},{3,5},{5,7},{7,9},{9,11},{11,13},{13,15},{15,17},{17,19},{19... | collective-permute-start | bytes 49160 | tf_op jit(solution)/shard_map/ppermute | solution.py:432
  60.1 6.1 %copy-start.2 = (bf16[8,96,256]{2,1,0:T(8,128)(2,1)S(1)}, bf16[8,96,256]{2,1,0:T(8,128)(2,1)}, u32[]{:S(2)}) copy-start(bf16[8,96,256]{2,1,0:T(8,128)(2,1)} %basis_ref.3) | copy-start | bytes 1179652
  60.2 6.1 %collective-permute-start.23 = (bf16[9,32,128]{2,1,0:T(8,128)(2,1)S(1)}, bf16[9,32,128]{2,1,0:T(8,128)(2,1)S(1)}, u32[]{:S(2)}, u32[]{:S(2)}) collective-permute-start(bf16[9,32,128]{2,1,0:T(8,128)(2,1)S(1)} %get-tuple-element.159), channel_id=1, source_target_pairs={{0,16},{1,17},{2,18},{3,19},{4,20},{5,21},{6,22},{7,23},{8,24},{9,... | collective-permute-start | bytes 221192 | tf_op jit(solution)/shard_map/ppermute | solution.py:265
  61.4 1.2 collective-permute-start.24
  61.4 1.3 %collective-permute-start.25 = (bf16[1,32,256]{2,1,0:T(8,128)(2,1)S(1)}, bf16[1,32,256]{2,1,0:T(8,128)(2,1)S(1)}, u32[]{:S(2)}, u32[]{:S(2)}) collective-permute-start(bf16[1,32,256]{2,1,0:T(8,128)(2,1)S(1)} %collective-permute-done.22), channel_id=1, source_target_pairs={{0,1},{1,0},{2,3},{3,2},{4,5},{5,4},{6,7},{7,6},{8,9},{9,8},{10,11... | collective-permute-start | bytes 49160 | tf_op jit(solution)/shard_map/ppermute | solution.py:274
  67.9 5.5 %collective-permute-start.26 = (bf16[9,32,128]{2,1,0:T(8,128)(2,1)S(1)}, bf16[9,32,128]{2,1,0:T(8,128)(2,1)S(1)}, u32[]{:S(2)}, u32[]{:S(2)}) collective-permute-start(bf16[9,32,128]{2,1,0:T(8,128)(2,1)S(1)} %get-tuple-element.166.refs_0_), channel_id=1, source_target_pairs={{0,16},{1,17},{2,18},{3,19},{4,20},{5,21},{6,22},{7,23},{8,24},{9,... | collective-permute-start | bytes 221192 | tf_op jit(solution)/shard_map/ppermute | solution.py:265
  73.4 6.5 %collective-permute-start.29 = (bf16[2,9,32,128]{3,2,1,0:T(8,128)(2,1)S(1)}, bf16[2,9,32,128]{3,2,1,0:T(8,128)(2,1)S(1)}, u32[]{:S(2)}, u32[]{:S(2)}) collective-permute-start(bf16[2,9,32,128]{3,2,1,0:T(8,128)(2,1)S(1)} %shard_map.107.refs_0_), channel_id=1, source_target_pairs={{0,8},{1,3},{2,10},{3,1},{4,12},{5,7},{6,14},{7,5},{8,0},{9,11},{1... | collective-permute-start | bytes 442376 | tf_op jit(solution)/shard_map/ppermute | solution.py:269
  73.5 6.8 %collective-permute-start.28 = (bf16[2,9,32,128]{3,2,1,0:T(8,128)(2,1)S(1)}, bf16[2,9,32,128]{3,2,1,0:T(8,128)(2,1)S(1)}, u32[]{:S(2)}, u32[]{:S(2)}) collective-permute-start(bf16[2,9,32,128]{3,2,1,0:T(8,128)(2,1)S(1)} %shard_map.107.refs_0_), channel_id=1, source_target_pairs={{0,4},{1,9},{2,6},{3,11},{4,0},{5,13},{6,2},{7,15},{8,12},{9,1},{1... | collective-permute-start | bytes 442376 | tf_op jit(solution)/shard_map/ppermute | solution.py:269
  74.9 5.4 %collective-permute-start.27 = (bf16[2,9,32,128]{3,2,1,0:T(8,128)(2,1)S(1)}, bf16[2,9,32,128]{3,2,1,0:T(8,128)(2,1)S(1)}, u32[]{:S(2)}, u32[]{:S(2)}) collective-permute-start(bf16[2,9,32,128]{3,2,1,0:T(8,128)(2,1)S(1)} %shard_map.107.refs_0_), channel_id=1, source_target_pairs={{0,2},{1,5},{2,0},{3,7},{4,6},{5,1},{6,4},{7,3},{8,10},{9,13},{10,... | collective-permute-start | bytes 442376 | tf_op jit(solution)/shard_map/ppermute | solution.py:269
  77.3 10.3 %collective-permute-start.33 = (bf16[2,9,32,128]{3,2,1,0:T(8,128)(2,1)S(1)}, bf16[2,9,32,128]{3,2,1,0:T(8,128)(2,1)S(1)}, u32[]{:S(2)}, u32[]{:S(2)}) collective-permute-start(bf16[2,9,32,128]{3,2,1,0:T(8,128)(2,1)S(1)} %shard_map.107.refs_0_), channel_id=1, source_target_pairs={{0,14},{1,15},{2,12},{3,13},{4,10},{5,11},{6,8},{7,9},{8,6},{9,7},... | collective-permute-start | bytes 442376 | tf_op jit(solution)/shard_map/ppermute | solution.py:269
  80.3 7.9 %collective-permute-start.30 = (bf16[2,9,32,128]{3,2,1,0:T(8,128)(2,1)S(1)}, bf16[2,9,32,128]{3,2,1,0:T(8,128)(2,1)S(1)}, u32[]{:S(2)}, u32[]{:S(2)}) collective-permute-start(bf16[2,9,32,128]{3,2,1,0:T(8,128)(2,1)S(1)} %collective-permute-done.27.refs_1_), channel_id=1, source_target_pairs={{0,4},{1,9},{2,6},{3,11},{4,0},{5,13},{6,2},{7,15},{8,12},{9,1},{1... | collective-permute-start | bytes 442376 | tf_op jit(solution)/shard_map/ppermute | solution.py:269
  81.4 6.3 %collective-permute-start.34 = (bf16[1,32,256]{2,1,0:T(8,128)(2,1)S(1)}, bf16[1,32,256]{2,1,0:T(8,128)(2,1)S(1)}, u32[]{:S(2)}, u32[]{:S(2)}) collective-permute-start(bf16[1,32,256]{2,1,0:T(8,128)(2,1)S(1)} %get-tuple-element.173), channel_id=1, source_target_pairs={{1,3},{3,5},{5,7},{7,9},{9,11},{11,13},{13,15},{15,17},{17,19},{19... | collective-permute-start | bytes 49160 | tf_op jit(solution)/shard_map/ppermute | solution.py:416
  82.6 7.6 %collective-permute-start.32 = (bf16[2,9,32,128]{3,2,1,0:T(8,128)(2,1)S(1)}, bf16[2,9,32,128]{3,2,1,0:T(8,128)(2,1)S(1)}, u32[]{:S(2)}, u32[]{:S(2)}) collective-permute-start(bf16[2,9,32,128]{3,2,1,0:T(8,128)(2,1)S(1)} %collective-permute-done.28.refs_2_), channel_id=1, source_target_pairs={{0,8},{1,3},{2,10},{3,1},{4,12},{5,7},{6,14},{7,5},{8,0},{9,11},{1... | collective-permute-start | bytes 442376 | tf_op jit(solution)/shard_map/ppermute | solution.py:269
  87.0 5.1 %collective-permute-start.31 = (bf16[2,9,32,128]{3,2,1,0:T(8,128)(2,1)S(1)}, bf16[2,9,32,128]{3,2,1,0:T(8,128)(2,1)S(1)}, u32[]{:S(2)}, u32[]{:S(2)}) collective-permute-start(bf16[2,9,32,128]{3,2,1,0:T(8,128)(2,1)S(1)} %collective-permute-done.29.refs_4_), channel_id=1, source_target_pairs={{0,2},{1,5},{2,0},{3,7},{4,6},{5,1},{6,4},{7,3},{8,10},{9,13},{10,... | collective-permute-start | bytes 442376 | tf_op jit(solution)/shard_map/ppermute | solution.py:269
  87.7 4.5 %collective-permute-start.35 = (bf16[2,9,32,128]{3,2,1,0:T(8,128)(2,1)S(1)}, bf16[2,9,32,128]{3,2,1,0:T(8,128)(2,1)S(1)}, u32[]{:S(2)}, u32[]{:S(2)}) collective-permute-start(bf16[2,9,32,128]{3,2,1,0:T(8,128)(2,1)S(1)} %shard_map.107.refs_0_), channel_id=1, source_target_pairs={{0,1},{1,0},{2,3},{3,2},{4,5},{5,4},{6,7},{7,6},{8,9},{9,8},{10,11... | collective-permute-start | bytes 442376 | tf_op jit(solution)/shard_map/ppermute | solution.py:274
  87.7 5.0 %collective-permute-start.36 = (bf16[2,9,32,128]{3,2,1,0:T(8,128)(2,1)S(1)}, bf16[2,9,32,128]{3,2,1,0:T(8,128)(2,1)S(1)}, u32[]{:S(2)}, u32[]{:S(2)}) collective-permute-start(bf16[2,9,32,128]{3,2,1,0:T(8,128)(2,1)S(1)} %collective-permute-done.27.refs_1_), channel_id=1, source_target_pairs={{0,1},{1,0},{2,3},{3,2},{4,5},{5,4},{6,7},{7,6},{8,9},{9,8},{10,11... | collective-permute-start | bytes 442376 | tf_op jit(solution)/shard_map/ppermute | solution.py:274
  88.2 4.5 %collective-permute-start.37 = (bf16[2,9,32,128]{3,2,1,0:T(8,128)(2,1)S(1)}, bf16[2,9,32,128]{3,2,1,0:T(8,128)(2,1)S(1)}, u32[]{:S(2)}, u32[]{:S(2)}) collective-permute-start(bf16[2,9,32,128]{3,2,1,0:T(8,128)(2,1)S(1)} %collective-permute-done.28.refs_2_), channel_id=1, source_target_pairs={{0,1},{1,0},{2,3},{3,2},{4,5},{5,4},{6,7},{7,6},{8,9},{9,8},{10,11... | collective-permute-start | bytes 442376 | tf_op jit(solution)/shard_map/ppermute | solution.py:274
  90.2 3.0 %collective-permute-start.39 = (bf16[2,9,32,128]{3,2,1,0:T(8,128)(2,1)S(1)}, bf16[2,9,32,128]{3,2,1,0:T(8,128)(2,1)S(1)}, u32[]{:S(2)}, u32[]{:S(2)}) collective-permute-start(bf16[2,9,32,128]{3,2,1,0:T(8,128)(2,1)S(1)} %collective-permute-done.29.refs_4_), channel_id=1, source_target_pairs={{0,1},{1,0},{2,3},{3,2},{4,5},{5,4},{6,7},{7,6},{8,9},{9,8},{10,11... | collective-permute-start | bytes 442376 | tf_op jit(solution)/shard_map/ppermute | solution.py:274
  92.1 1.4 %collective-permute-start.38 = (bf16[2,9,32,128]{3,2,1,0:T(8,128)(2,1)S(1)}, bf16[2,9,32,128]{3,2,1,0:T(8,128)(2,1)S(1)}, u32[]{:S(2)}, u32[]{:S(2)}) collective-permute-start(bf16[2,9,32,128]{3,2,1,0:T(8,128)(2,1)S(1)} %collective-permute-done.30.refs_3_), channel_id=1, source_target_pairs={{0,1},{1,0},{2,3},{3,2},{4,5},{5,4},{6,7},{7,6},{8,9},{9,8},{10,11... | collective-permute-start | bytes 442376 | tf_op jit(solution)/shard_map/ppermute | solution.py:274
  92.2 1.6 %collective-permute-start.40 = (bf16[2,9,32,128]{3,2,1,0:T(8,128)(2,1)S(1)}, bf16[2,9,32,128]{3,2,1,0:T(8,128)(2,1)S(1)}, u32[]{:S(2)}, u32[]{:S(2)}) collective-permute-start(bf16[2,9,32,128]{3,2,1,0:T(8,128)(2,1)S(1)} %collective-permute-done.31.refs_5_), channel_id=1, source_target_pairs={{0,1},{1,0},{2,3},{3,2},{4,5},{5,4},{6,7},{7,6},{8,9},{9,8},{10,11... | collective-permute-start | bytes 442376 | tf_op jit(solution)/shard_map/ppermute | solution.py:274
  92.7 1.4 %collective-permute-start.41 = (bf16[2,9,32,128]{3,2,1,0:T(8,128)(2,1)S(1)}, bf16[2,9,32,128]{3,2,1,0:T(8,128)(2,1)S(1)}, u32[]{:S(2)}, u32[]{:S(2)}) collective-permute-start(bf16[2,9,32,128]{3,2,1,0:T(8,128)(2,1)S(1)} %collective-permute-done.32.refs_6_), channel_id=1, source_target_pairs={{0,1},{1,0},{2,3},{3,2},{4,5},{5,4},{6,7},{7,6},{8,9},{9,8},{10,11... | collective-permute-start | bytes 442376 | tf_op jit(solution)/shard_map/ppermute | solution.py:274
  92.7 1.5 %collective-permute-start.42 = (bf16[2,9,32,128]{3,2,1,0:T(8,128)(2,1)S(1)}, bf16[2,9,32,128]{3,2,1,0:T(8,128)(2,1)S(1)}, u32[]{:S(2)}, u32[]{:S(2)}) collective-permute-start(bf16[2,9,32,128]{3,2,1,0:T(8,128)(2,1)S(1)} %collective-permute-done.33.refs_7_), channel_id=1, source_target_pairs={{0,1},{1,0},{2,3},{3,2},{4,5},{5,4},{6,7},{7,6},{8,9},{9,8},{10,11... | collective-permute-start | bytes 442376 | tf_op jit(solution)/shard_map/ppermute | solution.py:274
  97.7 2.1 %collective-permute-start.43 = (bf16[4,2,9,32,128]{4,3,2,1,0:T(8,128)(2,1)S(1)}, bf16[4,2,9,32,128]{4,3,2,1,0:T(8,128)(2,1)S(1)}, u32[]{:S(2)}, u32[]{:S(2)}) collective-permute-start(bf16[4,2,9,32,128]{4,3,2,1,0:T(8,128)(2,1)S(1)} %get-tuple-element.184), channel_id=1, source_target_pairs={{0,1},{1,0},{2,3},{3,2},{4,5},{5,4},{6,7},{7,6},{8,9},{9,8},{10,11... | collective-permute-start | bytes 1769480 | tf_op jit(solution)/shard_map/ppermute | solution.py:274
  99.9 10.1 %collective-permute-start.48 = (bf16[4,2,9,32,128]{4,3,2,1,0:T(8,128)(2,1)S(1)}, bf16[4,2,9,32,128]{4,3,2,1,0:T(8,128)(2,1)S(1)}, u32[]{:S(2)}, u32[]{:S(2)}) collective-permute-start(bf16[4,2,9,32,128]{4,3,2,1,0:T(8,128)(2,1)S(1)} %get-tuple-element.194), channel_id=1, source_target_pairs={{0,1},{1,0},{2,3},{3,2},{4,5},{5,4},{6,7},{7,6},{8,9},{9,8},{10,11... | collective-permute-start | bytes 1769480 | tf_op jit(solution)/shard_map/ppermute | solution.py:274
  100.3 6.4 %collective-permute-start.44 = (bf16[2,9,32,128]{3,2,1,0:T(8,128)(2,1)S(1)}, bf16[2,9,32,128]{3,2,1,0:T(8,128)(2,1)S(1)}, u32[]{:S(2)}, u32[]{:S(2)}) collective-permute-start(bf16[2,9,32,128]{3,2,1,0:T(8,128)(2,1)S(1)} %get-tuple-element.190), channel_id=1, source_target_pairs={{0,4},{1,9},{2,6},{3,11},{4,0},{5,13},{6,2},{7,15},{8,12},{9,1},{1... | collective-permute-start | bytes 442376 | tf_op jit(solution)/shard_map/ppermute | solution.py:269
  101.5 6.3 %collective-permute-start.45 = (bf16[2,9,32,128]{3,2,1,0:T(8,128)(2,1)S(1)}, bf16[2,9,32,128]{3,2,1,0:T(8,128)(2,1)S(1)}, u32[]{:S(2)}, u32[]{:S(2)}) collective-permute-start(bf16[2,9,32,128]{3,2,1,0:T(8,128)(2,1)S(1)} %get-tuple-element.191), channel_id=1, source_target_pairs={{0,8},{1,3},{2,10},{3,1},{4,12},{5,7},{6,14},{7,5},{8,0},{9,11},{1... | collective-permute-start | bytes 442376 | tf_op jit(solution)/shard_map/ppermute | solution.py:269
  102.1 6.7 %collective-permute-start.46 = (bf16[2,9,32,128]{3,2,1,0:T(8,128)(2,1)S(1)}, bf16[2,9,32,128]{3,2,1,0:T(8,128)(2,1)S(1)}, u32[]{:S(2)}, u32[]{:S(2)}) collective-permute-start(bf16[2,9,32,128]{3,2,1,0:T(8,128)(2,1)S(1)} %get-tuple-element.192), channel_id=1, source_target_pairs={{0,2},{1,5},{2,0},{3,7},{4,6},{5,1},{6,4},{7,3},{8,10},{9,13},{10,... | collective-permute-start | bytes 442376 | tf_op jit(solution)/shard_map/ppermute | solution.py:269
  102.8 7.3 %collective-permute-start.47 = (bf16[2,9,32,128]{3,2,1,0:T(8,128)(2,1)S(1)}, bf16[2,9,32,128]{3,2,1,0:T(8,128)(2,1)S(1)}, u32[]{:S(2)}, u32[]{:S(2)}) collective-permute-start(bf16[2,9,32,128]{3,2,1,0:T(8,128)(2,1)S(1)} %get-tuple-element.193), channel_id=1, source_target_pairs={{0,12},{1,11},{2,14},{3,9},{4,8},{5,15},{6,10},{7,13},{8,4},{9,3},... | collective-permute-start | bytes 442376 | tf_op jit(solution)/shard_map/ppermute | solution.py:269
  110.3 5.5 %collective-permute-start.49 = (bf16[2,9,32,128]{3,2,1,0:T(8,128)(2,1)S(1)}, bf16[2,9,32,128]{3,2,1,0:T(8,128)(2,1)S(1)}, u32[]{:S(2)}, u32[]{:S(2)}) collective-permute-start(bf16[2,9,32,128]{3,2,1,0:T(8,128)(2,1)S(1)} %get-tuple-element.207), channel_id=1, source_target_pairs={{0,2},{1,5},{2,0},{3,7},{4,6},{5,1},{6,4},{7,3},{8,10},{9,13},{10,... | collective-permute-start | bytes 442376 | tf_op jit(solution)/shard_map/ppermute | solution.py:269
  111.0 5.1 %collective-permute-start.50 = (bf16[2,9,32,128]{3,2,1,0:T(8,128)(2,1)S(1)}, bf16[2,9,32,128]{3,2,1,0:T(8,128)(2,1)S(1)}, u32[]{:S(2)}, u32[]{:S(2)}) collective-permute-start(bf16[2,9,32,128]{3,2,1,0:T(8,128)(2,1)S(1)} %get-tuple-element.208), channel_id=1, source_target_pairs={{0,4},{1,9},{2,6},{3,11},{4,0},{5,13},{6,2},{7,15},{8,12},{9,1},{1... | collective-permute-start | bytes 442376 | tf_op jit(solution)/shard_map/ppermute | solution.py:269
  111.8 5.1 %collective-permute-start.51 = (bf16[2,9,32,128]{3,2,1,0:T(8,128)(2,1)S(1)}, bf16[2,9,32,128]{3,2,1,0:T(8,128)(2,1)S(1)}, u32[]{:S(2)}, u32[]{:S(2)}) collective-permute-start(bf16[2,9,32,128]{3,2,1,0:T(8,128)(2,1)S(1)} %get-tuple-element.209), channel_id=1, source_target_pairs={{0,8},{1,3},{2,10},{3,1},{4,12},{5,7},{6,14},{7,5},{8,0},{9,11},{1... | collective-permute-start | bytes 442376 | tf_op jit(solution)/shard_map/ppermute | solution.py:269
  117.0 6.1 %collective-permute-start.52 = (bf16[9,32,128]{2,1,0:T(8,128)(2,1)S(1)}, bf16[9,32,128]{2,1,0:T(8,128)(2,1)S(1)}, u32[]{:S(2)}, u32[]{:S(2)}) collective-permute-start(bf16[9,32,128]{2,1,0:T(8,128)(2,1)S(1)} %get-tuple-element.216), channel_id=1, source_target_pairs={{0,16},{1,17},{2,18},{3,19},{4,20},{5,21},{6,22},{7,23},{8,24},{9,... | collective-permute-start | bytes 221192 | tf_op jit(solution)/shard_map/ppermute | solution.py:265
  119.8 1.2 collective-permute-start.53
  119.8 1.3 %collective-permute-start.54 = (bf16[1,32,256]{2,1,0:T(8,128)(2,1)S(1)}, bf16[1,32,256]{2,1,0:T(8,128)(2,1)S(1)}, u32[]{:S(2)}, u32[]{:S(2)}) collective-permute-start(bf16[1,32,256]{2,1,0:T(8,128)(2,1)S(1)} %collective-permute-done.34), channel_id=1, source_target_pairs={{0,1},{1,0},{2,3},{3,2},{4,5},{5,4},{6,7},{7,6},{8,9},{9,8},{10,11... | collective-permute-start | bytes 49160 | tf_op jit(solution)/shard_map/ppermute | solution.py:274
  (3 other events, 13.1 us)

commit v23 on v22

--- a/solution.py
+++ b/solution.py
@@ -93,7 +93,7 @@
     emit_coeffs(values, basis_ref, transfer_ref, ranks_ref, out_ref, copies[2].wait)
 
 
-def couple_kernel(source_ref, target_ref, coupling_ref, *refs, order, joined, unroll):
+def couple_kernel(source_ref, target_ref, coupling_ref, *refs, order, distant, joined, unroll):
     chips = sum(len(group) for group in order)
     in_refs, out_refs, (sources, total) = refs[: -2 - 2 * len(order)], refs[-2 - 2 * len(order) : -2], refs[-2:]
     blocks, rank_top, _ = coupling_ref.shape
@@ -101,8 +101,8 @@
     if joined:
         cores, in_refs = (in_refs[: len(in_refs) // 2], in_refs[len(in_refs) // 2 :]), []
         for near_pieces, *far_pieces in cores:
-            pieces = {chip: near_pieces.at[place] for place, chip in enumerate(order[1])}
-            pieces |= dict(zip(order[0], far_pieces))
+            pieces = {chip: near_pieces.at[place] for place, chip in enumerate(order[-1])}
+            pieces |= dict(zip(distant, far_pieces))
             in_refs += [pieces[chip] for chip in range(chips)]
     quads = mains // 3
     clusters = mains + quads
@@ -307,13 +307,14 @@
         ],
     )(ranks, charges, basis, transfer)
 
-    order = ((x | y | z, x | y, y | z, z | x), (0, x, y, z))
+    distant = (x | y, y | z, z | x, x | y | z)
+    order = (distant[:2], distant[2:], (0, x, y, z))
     def couple(joined, *args):
         return pl.pallas_call(
-            functools.partial(couple_kernel, order=order, joined=joined, unroll=blocks),
-            out_shape=[shape((4, far) + tile_shape, BF)] * 4,
+            functools.partial(couple_kernel, order=order, distant=distant, joined=joined, unroll=blocks),
+            out_shape=[shape((len(group), far) + tile_shape, BF) for group in order] * cores,
             in_specs=[SMEM, SMEM] + [VMEM] * (len(args) - 2),
-            out_specs=[VMEM] * 4,
+            out_specs=[VMEM] * (cores * len(order)),
             scratch_shapes=[
                 pltpu.VMEM((devices * clusters, rhs, LANES), BF),
                 pltpu.VMEM((devices * clusters, rhs, LANES), F32),
@@ -373,7 +374,7 @@
         out_specs=[VMEM],
         compiler_params=params(16),
     )
-    far_add = adder(add_kernel, 2, [part_shape] * 4)
+    far_add = adder(add_kernel, 2, [part_shape] * 2)
     join_near = adder(join_kernel, 4, [shape((4,) + part_shape.shape, BF)])
 
     def middle_add(*args):
@@ -405,8 +406,8 @@
         second_round = {x | y: swap(got[x], y), y | z: swap(got[y], z), z | x: swap(got[z], x)}
         if with_coeffs:
             second_round[x | y | z] = swap(got[x], y | z)
-            (near_pieces,) = join_near(*[got[chip] for chip in order[1]])
-            far_pieces, other_near = barrier(([second_round[chip] for chip in order[0]], swap_cores(near_pieces)))
+            (near_pieces,) = join_near(*[got[chip] for chip in order[-1]])
+            far_pieces, other_near = barrier(([second_round[chip] for chip in distant], swap_cores(near_pieces)))
             other_far = [swap_cores(part) for part in far_pieces]
             args = (near_pieces, *far_pieces, other_near, *other_far)
         else:
@@ -415,12 +416,14 @@
             got |= second_round
             got, corner, outer = barrier((got, corner, lax.ppermute(outer, "clu", halo_pairs)))
             got[x | y | z] = corner
-            other |= {chip: swap_cores(got[chip]) for chip in order[0]}
+            other |= {chip: swap_cores(got[chip]) for chip in distant}
             args = [got[chip] for chip in range(chips)] + [other[chip] for chip in range(chips)]
-        keep_long, keep, send_long, send = couple(with_coeffs, source_rows, target_rows, coupling, *args)
-
-        corner, xy, yz, zx = far_add(keep_long, swap_cores(send_long))
-        corner, xy, yz, zx, send = barrier((corner, xy, yz, zx, send))
+        totals = couple(with_coeffs, source_rows, target_rows, coupling, *args)
+        *keep_far, keep, send_first, send_second, send = totals
+
+        xy, yz = far_add(keep_far[0], swap_cores(send_first))
+        zx, corner = far_add(keep_far[1], swap_cores(send_second))
+        xy, yz, send = barrier((xy, yz, send))
         arrived = [swap(xy, y), swap(yz, z), swap(zx, x)]
         if not with_coeffs:
             arrived.append(swap(corner, y | z))

time: 125 us -> 127 us (1.016)
  waiting for transfers between devices: 49.2 us -> 55.6 us
  starting transfers between devices: 53 us -> 48.3 us
    ppermute x28, waiting for transfers between devices: 27 us -> 30.6 us  [swap(): lax.ppermute(part, 'clu', [(d, d ^ (turned if d % cores else direction) *...]
    ppermute x28, starting transfers between devices: 37 us -> 33.8 us  [swap(): lax.ppermute(part, 'clu', [(d, d ^ (turned if d % cores else direction) *...]
    ppermute x4, waiting for transfers between devices: 10.3 us -> 12.9 us  [swap_far(): lax.ppermute(part, 'clu', [(d, (d + shift * cube) % devices) for d in ran...]
    ppermute x4, starting transfers between devices: 8.47 us -> 6.34 us  [swap_far(): lax.ppermute(part, 'clu', [(d, (d + shift * cube) % devices) for d in ran...]
    ppermute x21 -> x23, starting transfers between devices: 5 us -> 5.6 us  [swap_cores(): return lax.ppermute(part, 'clu', [(d, d ^ 1) for d in range(devices)])]
    ppermute x21 -> x23, waiting for transfers between devices: 7.58 us -> 7.71 us  [swap_cores(): return lax.ppermute(part, 'clu', [(d, d ^ 1) for d in range(devices)])]
    pallas_call x5 -> x7, Pallas kernels: 7.24 us -> 7.25 us  [the longest x2 6.93 us: couple(): pl.pallas_call(functools.partial(couple_kernel, order=order, distant=dist...]
  transfers between devices with their start and end apart: 55 -> 57, of which waited for: 39 -> 41; matrix products, arithmetic and copies ran while one was open for 4% -> 4% of each run, Pallas kernels for 2% -> 2%
where the time goes in v23:
time: 127 us; the launch traced here: 126 us
  waiting for transfers between devices  55.6 us (44%)
  starting transfers between devices  48.3 us (38%)
  Pallas kernels  16 us (13%)
  local copies, waits for them, and re-layouts  5.63 us (4%)
    ppermute x28, starting transfers between devices, swap(): lax.ppermute(part, 'clu', [(d, d ^ (turned if d % cores else direction) *...  33.8 us
    ppermute x28, waiting for transfers between devices, swap(): lax.ppermute(part, 'clu', [(d, d ^ (turned if d % cores else direction) *...  30.6 us
    ppermute x4, waiting for transfers between devices, swap_far(): lax.ppermute(part, 'clu', [(d, (d + shift * cube) % devices) for d in ran...  12.9 us
    ppermute x23, waiting for transfers between devices, swap_cores(): return lax.ppermute(part, 'clu', [(d, d ^ 1) for d in range(devices)])  7.71 us
    pallas_call x2, Pallas kernels, couple(): pl.pallas_call(functools.partial(couple_kernel, order=order, distant=dist...  6.93 us
    ppermute x4, starting transfers between devices, swap_far(): lax.ppermute(part, 'clu', [(d, (d + shift * cube) % devices) for d in ran...  6.34 us
    unnamed x25, local copies, waits for them, and re-layouts  5.63 us
    ppermute x23, starting transfers between devices, swap_cores(): return lax.ppermute(part, 'clu', [(d, d ^ 1) for d in range(devices)])  5.6 us
  transfers between devices with their start and end apart: 57, of which 41 were waited for; matrix products, arithmetic and copies ran while one was open for 4% of the time, Pallas kernels for 2%

profile of v23, /device:TPU:0, one launch (start us, length us, event | category | flops | bytes accessed | tf_op | source)
XLA Modules:
  0.0 126.4 jit_solution(2566272644529135048)
XLA Ops:
  0.6 2.9 %shard_map.95 = (bf16[9,32,128]{2,1,0:T(8,128)(2,1)}, bf16[1,32,256]{2,1,0:T(8,128)(2,1)}, bf16[1,32,256]{2,1,0:T(8,128)(2,1)}) custom-call(s32[12]{0:T(128)} %ranks_ref.5, bf16[8,32,256]{2,1,0:T(8,128)(2,1)} %v_ref.1, bf16[8,96,256]{2,1,0:T(8,128)(2,1)} %basis_ref.3, bf16[8,96,96]{2,1,0:T(8,128)(2,1)} %transfer_ref.3), custom_call_target="tpu_custom_call" | custom-call | tf_op jit(solution)/shard_map/pallas_call | solution.py:297
  3.6 4.1 %collective-permute-start = (bf16[9,32,128]{2,1,0:T(8,128)(2,1)}, bf16[9,32,128]{2,1,0:T(8,128)(2,1)S(1)}, u32[]{:S(2)}, u32[]{:S(2)}) collective-permute-start(bf16[9,32,128]{2,1,0:T(8,128)(2,1)} %get-tuple-element.112.__.refs_0_), channel_id=1, source_target_pairs={{0,16},{1,17},{2,18},{3,19},{4,20},{5,21},{6,22},{7,23},{8,24},{9,... | collective-permute-start | bytes 221192 | tf_op jit(solution)/shard_map/ppermute | solution.py:265
  7.7 4.8 %copy.10._.coupling_ref = bf16[128,96,96]{2,1,0:T(8,128)(2,1)} copy(bf16[128,96,96]{0,2,1:T(8,128)(2,1)} %param.12) | data formatting | bytes 4718592 | tf_op args[4]
  12.4 0.6 shard_map.96._
  13.0 0.8 copy-done.6
  13.9 1.6 %collective-permute-start.3 = (bf16[2,9,32,128]{3,2,1,0:T(8,128)(2,1)S(1)}, bf16[2,9,32,128]{3,2,1,0:T(8,128)(2,1)S(1)}, u32[]{:S(2)}, u32[]{:S(2)}) collective-permute-start(bf16[2,9,32,128]{3,2,1,0:T(8,128)(2,1)S(1)} %shard_map.97.refs_0_), channel_id=1, source_target_pairs={{0,8},{1,3},{2,10},{3,1},{4,12},{5,7},{6,14},{7,5},{8,0},{9,11},{1... | collective-permute-start | bytes 442376 | tf_op jit(solution)/shard_map/ppermute | solution.py:269
  15.5 1.5 %collective-permute-start.2 = (bf16[2,9,32,128]{3,2,1,0:T(8,128)(2,1)S(1)}, bf16[2,9,32,128]{3,2,1,0:T(8,128)(2,1)S(1)}, u32[]{:S(2)}, u32[]{:S(2)}) collective-permute-start(bf16[2,9,32,128]{3,2,1,0:T(8,128)(2,1)S(1)} %shard_map.97.refs_0_), channel_id=1, source_target_pairs={{0,4},{1,9},{2,6},{3,11},{4,0},{5,13},{6,2},{7,15},{8,12},{9,1},{1... | collective-permute-start | bytes 442376 | tf_op jit(solution)/shard_map/ppermute | solution.py:269
  17.0 1.5 %collective-permute-start.1 = (bf16[2,9,32,128]{3,2,1,0:T(8,128)(2,1)S(1)}, bf16[2,9,32,128]{3,2,1,0:T(8,128)(2,1)S(1)}, u32[]{:S(2)}, u32[]{:S(2)}) collective-permute-start(bf16[2,9,32,128]{3,2,1,0:T(8,128)(2,1)S(1)} %shard_map.97.refs_0_), channel_id=1, source_target_pairs={{0,2},{1,5},{2,0},{3,7},{4,6},{5,1},{6,4},{7,3},{8,10},{9,13},{10,... | collective-permute-start | bytes 442376 | tf_op jit(solution)/shard_map/ppermute | solution.py:269
  18.5 0.6 shard_map.98.near_ref
  19.1 1.3 %collective-permute-done.3.refs_3_ = bf16[2,9,32,128]{3,2,1,0:T(8,128)(2,1)S(1)} collective-permute-done((bf16[2,9,32,128]{3,2,1,0:T(8,128)(2,1)S(1)}, bf16[2,9,32,128]{3,2,1,0:T(8,128)(2,1)S(1)}, u32[]{:S(2)}, u32[]{:S(2)}) %collective-permute-start.3) | collective-permute-done | bytes 147488 | tf_op jit(solution)/shard_map/ppermute | solution.py:269
  20.5 1.3 %collective-permute-done.2.refs_2_ = bf16[2,9,32,128]{3,2,1,0:T(8,128)(2,1)S(1)} collective-permute-done((bf16[2,9,32,128]{3,2,1,0:T(8,128)(2,1)S(1)}, bf16[2,9,32,128]{3,2,1,0:T(8,128)(2,1)S(1)}, u32[]{:S(2)}, u32[]{:S(2)}) %collective-permute-start.2) | collective-permute-done | bytes 147488 | tf_op jit(solution)/shard_map/ppermute | solution.py:269
  22.3 0.5 collective-permute-start.5
  22.8 1.5 %collective-permute-start.6 = (bf16[2,9,32,128]{3,2,1,0:T(8,128)(2,1)S(1)}, bf16[2,9,32,128]{3,2,1,0:T(8,128)(2,1)S(1)}, u32[]{:S(2)}, u32[]{:S(2)}) collective-permute-start(bf16[2,9,32,128]{3,2,1,0:T(8,128)(2,1)S(1)} %collective-permute-done.3.refs_3_), channel_id=1, source_target_pairs={{0,2},{1,5},{2,0},{3,7},{4,6},{5,1},{6,4},{7,3},{8,10},{9,13},{10,... | collective-permute-start | bytes 442376 | tf_op jit(solution)/shard_map/ppermute | solution.py:269
  24.3 1.5 %collective-permute-start.7 = (bf16[2,9,32,128]{3,2,1,0:T(8,128)(2,1)S(1)}, bf16[2,9,32,128]{3,2,1,0:T(8,128)(2,1)S(1)}, u32[]{:S(2)}, u32[]{:S(2)}) collective-permute-start(bf16[2,9,32,128]{3,2,1,0:T(8,128)(2,1)S(1)} %collective-permute-done.1.refs_1_), channel_id=1, source_target_pairs={{0,12},{1,11},{2,14},{3,9},{4,8},{5,15},{6,10},{7,13},{8,4},{9,3},... | collective-permute-start | bytes 442376 | tf_op jit(solution)/shard_map/ppermute | solution.py:269
  25.8 1.5 %collective-permute-start.4 = (bf16[2,9,32,128]{3,2,1,0:T(8,128)(2,1)S(1)}, bf16[2,9,32,128]{3,2,1,0:T(8,128)(2,1)S(1)}, u32[]{:S(2)}, u32[]{:S(2)}) collective-permute-start(bf16[2,9,32,128]{3,2,1,0:T(8,128)(2,1)S(1)} %collective-permute-done.1.refs_1_), channel_id=1, source_target_pairs={{0,4},{1,9},{2,6},{3,11},{4,0},{5,13},{6,2},{7,15},{8,12},{9,1},{1... | collective-permute-start | bytes 442376 | tf_op jit(solution)/shard_map/ppermute | solution.py:269
  27.6 1.8 %collective-permute-done.6.refs_3_ = bf16[2,9,32,128]{3,2,1,0:T(8,128)(2,1)S(1)} collective-permute-done((bf16[2,9,32,128]{3,2,1,0:T(8,128)(2,1)S(1)}, bf16[2,9,32,128]{3,2,1,0:T(8,128)(2,1)S(1)}, u32[]{:S(2)}, u32[]{:S(2)}) %collective-permute-start.6) | collective-permute-done | bytes 147488 | tf_op jit(solution)/shard_map/ppermute | solution.py:269
  29.4 2.5 %collective-permute-done.7.refs_4_ = bf16[2,9,32,128]{3,2,1,0:T(8,128)(2,1)S(1)} collective-permute-done((bf16[2,9,32,128]{3,2,1,0:T(8,128)(2,1)S(1)}, bf16[2,9,32,128]{3,2,1,0:T(8,128)(2,1)S(1)}, u32[]{:S(2)}, u32[]{:S(2)}) %collective-permute-start.7) | collective-permute-done | bytes 147488 | tf_op jit(solution)/shard_map/ppermute | solution.py:269
  34.3 3.5 %shard_map.101 = (bf16[2,2,9,32,128]{4,3,2,1,0:T(8,128)(2,1)S(1)}, bf16[2,2,9,32,128]{4,3,2,1,0:T(8,128)(2,1)S(1)}, bf16[4,2,9,32,128]{4,3,2,1,0:T(8,128)(2,1)S(...) custom-call(s32[128]{0:T(128)S(1)} %bitcast.4, ...), custom_call_target="tpu_custom_call" | custom-call | flops 75497472 | bytes 10485760 | tf_op jit(solution)/shard_map/pallas_call | solution.py:313
  38.2 1.3 %collective-permute-done.13.swap_ref = bf16[2,2,9,32,128]{4,3,2,1,0:T(8,128)(2,1)S(1)} collective-permute-done((bf16[2,2,9,32,128]{4,3,2,1,0:T(8,128)(2,1)S(1)}, bf16[2,2,9,32,128]{4,3,2,1,0:T(8,128)(2,1)S(1)}, u32[]{:S(2)}, u32[]{:S(2)}) %collective-permute-start.13) | collective-permute-done | bytes 294944 | tf_op jit(solution)/shard_map/ppermute | solution.py:274
  40.1 1.0 collective-permute-start.14
  41.1 1.0 collective-permute-start.15
  42.3 1.0 collective-permute-start.17
  43.3 1.9 %collective-permute-start.22 = (bf16[2,9,32,128]{3,2,1,0:T(8,128)(2,1)S(1)}, bf16[2,9,32,128]{3,2,1,0:T(8,128)(2,1)S(1)}, u32[]{:S(2)}, u32[]{:S(2)}) collective-permute-start(bf16[2,9,32,128]{3,2,1,0:T(8,128)(2,1)S(1)} %get-tuple-element.151), channel_id=1, source_target_pairs={{0,14},{1,15},{2,12},{3,13},{4,10},{5,11},{6,8},{7,9},{8,6},{9,7},... | collective-permute-start | bytes 442376 | tf_op jit(solution)/shard_map/ppermute | solution.py:269
  45.4 0.9 collective-permute-done.15.refs_1_
  46.3 4.3 %collective-permute-done.17.refs_2_ = bf16[2,9,32,128]{3,2,1,0:T(8,128)(2,1)S(1)} collective-permute-done((bf16[2,9,32,128]{3,2,1,0:T(8,128)(2,1)S(1)}, bf16[2,9,32,128]{3,2,1,0:T(8,128)(2,1)S(1)}, u32[]{:S(2)}, u32[]{:S(2)}) %collective-permute-start.17) | collective-permute-done | bytes 147488 | tf_op jit(solution)/shard_map/ppermute | solution.py:269
  50.8 1.0 collective-permute-start.19
  51.9 1.1 collective-permute-start.20
  53.0 1.0 collective-permute-start.21
  54.0 1.3 %collective-permute-start.23 = (bf16[1,32,256]{2,1,0:T(8,128)(2,1)S(1)}, bf16[1,32,256]{2,1,0:T(8,128)(2,1)S(1)}, u32[]{:S(2)}, u32[]{:S(2)}) collective-permute-start(bf16[1,32,256]{2,1,0:T(8,128)(2,1)S(1)} %copy-done.11), channel_id=1, source_target_pairs={{1,3},{3,5},{5,7},{7,9},{9,11},{11,13},{13,15},{15,17},{17,19},{19... | collective-permute-start | bytes 49160 | tf_op jit(solution)/shard_map/ppermute | solution.py:435
  55.3 4.3 %collective-permute-done.23 = bf16[1,32,256]{2,1,0:T(8,128)(2,1)S(1)} collective-permute-done((bf16[1,32,256]{2,1,0:T(8,128)(2,1)S(1)}, bf16[1,32,256]{2,1,0:T(8,128)(2,1)S(1)}, u32[]{:S(2)}, u32[]{:S(2)}) %collective-permute-start.23) | collective-permute-done | bytes 16416 | tf_op jit(solution)/shard_map/ppermute | solution.py:435
  59.8 1.4 %collective-permute-start.24 = (bf16[9,32,128]{2,1,0:T(8,128)(2,1)S(1)}, bf16[9,32,128]{2,1,0:T(8,128)(2,1)S(1)}, u32[]{:S(2)}, u32[]{:S(2)}) collective-permute-start(bf16[9,32,128]{2,1,0:T(8,128)(2,1)S(1)} %get-tuple-element.159), channel_id=1, source_target_pairs={{0,16},{1,17},{2,18},{3,19},{4,20},{5,21},{6,22},{7,23},{8,24},{9,... | collective-permute-start | bytes 221192 | tf_op jit(solution)/shard_map/ppermute | solution.py:265
  61.2 0.5 collective-permute-start.26
  61.7 0.7 collective-permute-done.25.inner_ref
  62.7 3.2 %collective-permute-done.24.rest_0_ = bf16[9,32,128]{2,1,0:T(8,128)(2,1)S(1)} collective-permute-done((bf16[9,32,128]{2,1,0:T(8,128)(2,1)S(1)}, bf16[9,32,128]{2,1,0:T(8,128)(2,1)S(1)}, u32[]{:S(2)}, u32[]{:S(2)}) %collective-permute-start.24) | collective-permute-done | bytes 73760 | tf_op jit(solution)/shard_map/ppermute | solution.py:265
  65.9 1.6 %shard_map.107 = (bf16[8,32,256]{2,1,0:T(8,128)(2,1)}, bf16[9,32,128]{2,1,0:T(8,128)(2,1)S(1)}, bf16[1,32,256]{2,1,0:T(8,128)(2,1)S(1)}, bf16[1,32,256]{2,1,0:T(8,128)(2,1)S(1)}, bf16[8,32,256]{2,1,0:T(8,128)(2,1)S(1)}) custom-call(s32[12]{0:T(128)S(1)} %copy-done.7, f32[8,32,256]{2,1,0:T(8,128)S(1)} %shard_map.98.near_ref, ...), custom_call_target="tpu_custom_call" | custom-call | tf_op jit(solution)/shard_map/pallas_call | solution.py:441
  67.5 0.7 collective-permute-start.27
  68.1 5.1 %collective-permute-done.27.refs_1_ = bf16[9,32,128]{2,1,0:T(8,128)(2,1)S(1)} collective-permute-done((bf16[9,32,128]{2,1,0:T(8,128)(2,1)S(1)}, bf16[9,32,128]{2,1,0:T(8,128)(2,1)S(1)}, u32[]{:S(2)}, u32[]{:S(2)}) %collective-permute-start.27) | collective-permute-done | bytes 73760 | tf_op jit(solution)/shard_map/ppermute | solution.py:265
  73.4 1.0 collective-permute-start.29
  74.3 2.8 %collective-permute-start.28 = (bf16[2,9,32,128]{3,2,1,0:T(8,128)(2,1)S(1)}, bf16[2,9,32,128]{3,2,1,0:T(8,128)(2,1)S(1)}, u32[]{:S(2)}, u32[]{:S(2)}) collective-permute-start(bf16[2,9,32,128]{3,2,1,0:T(8,128)(2,1)S(1)} %shard_map.108.refs_0_), channel_id=1, source_target_pairs={{0,2},{1,5},{2,0},{3,7},{4,6},{5,1},{6,4},{7,3},{8,10},{9,13},{10,... | collective-permute-start | bytes 442376 | tf_op jit(solution)/shard_map/ppermute | solution.py:269
  77.1 0.6 shard_map.109.near_ref
  77.7 1.2 collective-permute-start.34
  78.9 1.1 collective-permute-done.30.refs_4_
  80.2 1.4 %collective-permute-done.28.refs_1_ = bf16[2,9,32,128]{3,2,1,0:T(8,128)(2,1)S(1)} collective-permute-done((bf16[2,9,32,128]{3,2,1,0:T(8,128)(2,1)S(1)}, bf16[2,9,32,128]{3,2,1,0:T(8,128)(2,1)S(1)}, u32[]{:S(2)}, u32[]{:S(2)}) %collective-permute-start.28) | collective-permute-done | bytes 147488 | tf_op jit(solution)/shard_map/ppermute | solution.py:269
  81.6 1.3 %collective-permute-start.35 = (bf16[1,32,256]{2,1,0:T(8,128)(2,1)S(1)}, bf16[1,32,256]{2,1,0:T(8,128)(2,1)S(1)}, u32[]{:S(2)}, u32[]{:S(2)}) collective-permute-start(bf16[1,32,256]{2,1,0:T(8,128)(2,1)S(1)} %get-tuple-element.173), channel_id=1, source_target_pairs={{1,3},{3,5},{5,7},{7,9},{9,11},{11,13},{13,15},{15,17},{17,19},{19... | collective-permute-start | bytes 49160 | tf_op jit(solution)/shard_map/ppermute | solution.py:417
  82.9 6.1 %collective-permute-start.33 = (bf16[2,9,32,128]{3,2,1,0:T(8,128)(2,1)S(1)}, bf16[2,9,32,128]{3,2,1,0:T(8,128)(2,1)S(1)}, u32[]{:S(2)}, u32[]{:S(2)}) collective-permute-start(bf16[2,9,32,128]{3,2,1,0:T(8,128)(2,1)S(1)} %collective-permute-done.29.refs_2_), channel_id=1, source_target_pairs={{0,8},{1,3},{2,10},{3,1},{4,12},{5,7},{6,14},{7,5},{8,0},{9,11},{1... | collective-permute-start | bytes 442376 | tf_op jit(solution)/shard_map/ppermute | solution.py:269
  89.5 2.6 %collective-permute-done.33.refs_6_ = bf16[2,9,32,128]{3,2,1,0:T(8,128)(2,1)S(1)} collective-permute-done((bf16[2,9,32,128]{3,2,1,0:T(8,128)(2,1)S(1)}, bf16[2,9,32,128]{3,2,1,0:T(8,128)(2,1)S(1)}, u32[]{:S(2)}, u32[]{:S(2)}) %collective-permute-start.33) | collective-permute-done | bytes 147488 | tf_op jit(solution)/shard_map/ppermute | solution.py:269
  92.1 1.9 %collective-permute-done.32.refs_5_ = bf16[2,9,32,128]{3,2,1,0:T(8,128)(2,1)S(1)} collective-permute-done((bf16[2,9,32,128]{3,2,1,0:T(8,128)(2,1)S(1)}, bf16[2,9,32,128]{3,2,1,0:T(8,128)(2,1)S(1)}, u32[]{:S(2)}, u32[]{:S(2)}) %collective-permute-start.32) | collective-permute-done | bytes 147488 | tf_op jit(solution)/shard_map/ppermute | solution.py:269
  94.1 0.5 collective-permute-start.41
  96.1 3.5 %shard_map.110 = (bf16[2,2,9,32,128]{4,3,2,1,0:T(8,128)(2,1)S(1)}, bf16[2,2,9,32,128]{4,3,2,1,0:T(8,128)(2,1)S(1)}, bf16[4,2,9,32,128]{4,3,2,1,0:T(8,128)(2,1)S(...) custom-call(s32[128]{0:T(128)S(1)} %bitcast.5, ...), custom_call_target="tpu_custom_call" | custom-call | flops 75497472 | bytes 10485760 | tf_op jit(solution)/shard_map/pallas_call | solution.py:313
  100.0 1.3 %collective-permute-done.44.swap_ref = bf16[2,2,9,32,128]{4,3,2,1,0:T(8,128)(2,1)S(1)} collective-permute-done((bf16[2,2,9,32,128]{4,3,2,1,0:T(8,128)(2,1)S(1)}, bf16[2,2,9,32,128]{4,3,2,1,0:T(8,128)(2,1)S(1)}, u32[]{:S(2)}, u32[]{:S(2)}) %collective-permute-start.44) | collective-permute-done | bytes 294944 | tf_op jit(solution)/shard_map/ppermute | solution.py:274
  101.9 0.6 collective-permute-start.46
  102.5 1.3 %collective-permute-done.47.swap_ref = bf16[2,2,9,32,128]{4,3,2,1,0:T(8,128)(2,1)S(1)} collective-permute-done((bf16[2,2,9,32,128]{4,3,2,1,0:T(8,128)(2,1)S(1)}, bf16[2,2,9,32,128]{4,3,2,1,0:T(8,128)(2,1)S(1)}, u32[]{:S(2)}, u32[]{:S(2)}) %collective-permute-start.47) | collective-permute-done | bytes 294944 | tf_op jit(solution)/shard_map/ppermute | solution.py:274
  104.0 1.6 %collective-permute-start.49 = (bf16[2,9,32,128]{3,2,1,0:T(8,128)(2,1)S(1)}, bf16[2,9,32,128]{3,2,1,0:T(8,128)(2,1)S(1)}, u32[]{:S(2)}, u32[]{:S(2)}) collective-permute-start(bf16[2,9,32,128]{3,2,1,0:T(8,128)(2,1)S(1)} %get-tuple-element.193), channel_id=1, source_target_pairs={{0,12},{1,11},{2,14},{3,9},{4,8},{5,15},{6,10},{7,13},{8,4},{9,3},... | collective-permute-start | bytes 442376 | tf_op jit(solution)/shard_map/ppermute | solution.py:269
  105.6 1.6 %collective-permute-done.45.refs_0_ = bf16[2,9,32,128]{3,2,1,0:T(8,128)(2,1)S(1)} collective-permute-done((bf16[2,9,32,128]{3,2,1,0:T(8,128)(2,1)S(1)}, bf16[2,9,32,128]{3,2,1,0:T(8,128)(2,1)S(1)}, u32[]{:S(2)}, u32[]{:S(2)}) %collective-permute-start.45) | collective-permute-done | bytes 147488 | tf_op jit(solution)/shard_map/ppermute | solution.py:269
  107.2 1.4 %collective-permute-done.46.refs_1_ = bf16[2,9,32,128]{3,2,1,0:T(8,128)(2,1)S(1)} collective-permute-done((bf16[2,9,32,128]{3,2,1,0:T(8,128)(2,1)S(1)}, bf16[2,9,32,128]{3,2,1,0:T(8,128)(2,1)S(1)}, u32[]{:S(2)}, u32[]{:S(2)}) %collective-permute-start.46) | collective-permute-done | bytes 147488 | tf_op jit(solution)/shard_map/ppermute | solution.py:269
  108.6 2.1 %collective-permute-done.48.refs_2_ = bf16[2,9,32,128]{3,2,1,0:T(8,128)(2,1)S(1)} collective-permute-done((bf16[2,9,32,128]{3,2,1,0:T(8,128)(2,1)S(1)}, bf16[2,9,32,128]{3,2,1,0:T(8,128)(2,1)S(1)}, u32[]{:S(2)}, u32[]{:S(2)}) %collective-permute-start.48) | collective-permute-done | bytes 147488 | tf_op jit(solution)/shard_map/ppermute | solution.py:269
  110.7 1.0 collective-permute-done.49.refs_3_
  111.9 1.1 collective-permute-start.51
  113.4 1.1 collective-permute-start.53
  114.5 3.6 %collective-permute-done.51.refs_0_ = bf16[2,9,32,128]{3,2,1,0:T(8,128)(2,1)S(1)} collective-permute-done((bf16[2,9,32,128]{3,2,1,0:T(8,128)(2,1)S(1)}, bf16[2,9,32,128]{3,2,1,0:T(8,128)(2,1)S(1)}, u32[]{:S(2)}, u32[]{:S(2)}) %collective-permute-start.51) | collective-permute-done | bytes 147488 | tf_op jit(solution)/shard_map/ppermute | solution.py:269
  118.7 0.5 collective-permute-start.56
  119.3 0.7 collective-permute-done.55.inner_ref
  120.2 4.5 %collective-permute-done.54.rest_0_ = bf16[9,32,128]{2,1,0:T(8,128)(2,1)S(1)} collective-permute-done((bf16[9,32,128]{2,1,0:T(8,128)(2,1)S(1)}, bf16[9,32,128]{2,1,0:T(8,128)(2,1)S(1)}, u32[]{:S(2)}, u32[]{:S(2)}) %collective-permute-start.54) | collective-permute-done | bytes 73760 | tf_op jit(solution)/shard_map/ppermute | solution.py:265
  124.8 1.6 %shard_map.116 = bf16[8,32,256]{2,1,0:T(8,128)(2,1)} custom-call(s32[12]{0:T(128)S(1)} %copy-done.7, f32[8,32,256]{2,1,0:T(8,128)S(1)} %shard_map.109.near_ref, f32[2,32,256]{2,1,0:T(8,128)S(1)} %shard_map.115.edge_ref, bf16[8,96,256]{2,1,0:T(8,128)(2,1)S(1)} %copy-done.2, bf16[8,96,96]{2,1,0:T(8,128)(2,1)S(1)} %copy-done.3, ...), custom_call_target="tpu_custom_call" | custom-call | tf_op jit(solution)/shard_map/pallas_call | solution.py:441
  (97 shorter events, 10.3 us)
Async XLA Ops:
  3.5 15.0 %copy-start = (bf16[8,3,256,256]{3,2,1,0:T(8,128)(2,1)S(1)}, bf16[8,3,256,256]{3,2,1,0:T(8,128)(2,1)}, u32[]{:S(2)}) copy-start(bf16[8,3,256,256]{3,2,1,0:T(8,128)(2,1)} %last_ref.3) | copy-start | bytes 9437188
  3.6 15.0 %copy-start.4 = (bf16[8,32,256]{2,1,0:T(8,128)(2,1)S(1)}, bf16[8,32,256]{2,1,0:T(8,128)(2,1)}, u32[]{:S(2)}) copy-start(bf16[8,32,256]{2,1,0:T(8,128)(2,1)} %v_ref.1) | copy-start | bytes 393220
  3.6 9.5 %collective-permute-start = (bf16[9,32,128]{2,1,0:T(8,128)(2,1)}, bf16[9,32,128]{2,1,0:T(8,128)(2,1)S(1)}, u32[]{:S(2)}, u32[]{:S(2)}) collective-permute-start(bf16[9,32,128]{2,1,0:T(8,128)(2,1)} %get-tuple-element.112.__.refs_0_), channel_id=1, source_target_pairs={{0,16},{1,17},{2,18},{3,19},{4,20},{5,21},{6,22},{7,23},{8,24},{9,... | collective-permute-start | bytes 221192 | tf_op jit(solution)/shard_map/ppermute | solution.py:265
  13.0 21.3 %copy-start.1 = (bf16[128,96,96]{2,1,0:T(8,128)(2,1)S(1)}, bf16[128,96,96]{2,1,0:T(8,128)(2,1)}, u32[]{:S(2)}) copy-start(bf16[128,96,96]{2,1,0:T(8,128)(2,1)} %copy.10._.coupling_ref) | copy-start | bytes 7077892
  13.8 19.4 %copy-start.8 = (s32[128]{0:T(128)S(1)}, s32[128]{0:T(128)}, u32[]{:S(2)}) copy-start(s32[128]{0:T(128)} %param.14) | copy-start | bytes 1540
  13.8 19.4 %copy-start.9 = (s32[128]{0:T(128)S(1)}, s32[128]{0:T(128)}, u32[]{:S(2)}) copy-start(s32[128]{0:T(128)} %param.15) | copy-start | bytes 1540
  13.9 6.6 %collective-permute-start.3 = (bf16[2,9,32,128]{3,2,1,0:T(8,128)(2,1)S(1)}, bf16[2,9,32,128]{3,2,1,0:T(8,128)(2,1)S(1)}, u32[]{:S(2)}, u32[]{:S(2)}) collective-permute-start(bf16[2,9,32,128]{3,2,1,0:T(8,128)(2,1)S(1)} %shard_map.97.refs_0_), channel_id=1, source_target_pairs={{0,8},{1,3},{2,10},{3,1},{4,12},{5,7},{6,14},{7,5},{8,0},{9,11},{1... | collective-permute-start | bytes 442376 | tf_op jit(solution)/shard_map/ppermute | solution.py:269
  15.5 6.2 %collective-permute-start.2 = (bf16[2,9,32,128]{3,2,1,0:T(8,128)(2,1)S(1)}, bf16[2,9,32,128]{3,2,1,0:T(8,128)(2,1)S(1)}, u32[]{:S(2)}, u32[]{:S(2)}) collective-permute-start(bf16[2,9,32,128]{3,2,1,0:T(8,128)(2,1)S(1)} %shard_map.97.refs_0_), channel_id=1, source_target_pairs={{0,4},{1,9},{2,6},{3,11},{4,0},{5,13},{6,2},{7,15},{8,12},{9,1},{1... | collective-permute-start | bytes 442376 | tf_op jit(solution)/shard_map/ppermute | solution.py:269
  17.0 5.1 %collective-permute-start.1 = (bf16[2,9,32,128]{3,2,1,0:T(8,128)(2,1)S(1)}, bf16[2,9,32,128]{3,2,1,0:T(8,128)(2,1)S(1)}, u32[]{:S(2)}, u32[]{:S(2)}) collective-permute-start(bf16[2,9,32,128]{3,2,1,0:T(8,128)(2,1)S(1)} %shard_map.97.refs_0_), channel_id=1, source_target_pairs={{0,2},{1,5},{2,0},{3,7},{4,6},{5,1},{6,4},{7,3},{8,10},{9,13},{10,... | collective-permute-start | bytes 442376 | tf_op jit(solution)/shard_map/ppermute | solution.py:269
  22.2 10.0 %collective-permute-start.8 = (bf16[4,2,9,32,128]{4,3,2,1,0:T(8,128)(2,1)S(1)}, bf16[4,2,9,32,128]{4,3,2,1,0:T(8,128)(2,1)S(1)}, u32[]{:S(2)}, u32[]{:S(2)}) collective-permute-start(bf16[4,2,9,32,128]{4,3,2,1,0:T(8,128)(2,1)S(1)} %shard_map.100.refs_0_), channel_id=1, source_target_pairs={{0,1},{1,0},{2,3},{3,2},{4,5},{5,4},{6,7},{7,6},{8,9},{9,8},{10,11... | collective-permute-start | bytes 1769480 | tf_op jit(solution)/shard_map/ppermute | solution.py:274
  22.3 5.3 %collective-permute-start.5 = (bf16[2,9,32,128]{3,2,1,0:T(8,128)(2,1)S(1)}, bf16[2,9,32,128]{3,2,1,0:T(8,128)(2,1)S(1)}, u32[]{:S(2)}, u32[]{:S(2)}) collective-permute-start(bf16[2,9,32,128]{3,2,1,0:T(8,128)(2,1)S(1)} %collective-permute-done.2.refs_2_), channel_id=1, source_target_pairs={{0,8},{1,3},{2,10},{3,1},{4,12},{5,7},{6,14},{7,5},{8,0},{9,11},{1... | collective-permute-start | bytes 442376 | tf_op jit(solution)/shard_map/ppermute | solution.py:269
  22.8 6.6 %collective-permute-start.6 = (bf16[2,9,32,128]{3,2,1,0:T(8,128)(2,1)S(1)}, bf16[2,9,32,128]{3,2,1,0:T(8,128)(2,1)S(1)}, u32[]{:S(2)}, u32[]{:S(2)}) collective-permute-start(bf16[2,9,32,128]{3,2,1,0:T(8,128)(2,1)S(1)} %collective-permute-done.3.refs_3_), channel_id=1, source_target_pairs={{0,2},{1,5},{2,0},{3,7},{4,6},{5,1},{6,4},{7,3},{8,10},{9,13},{10,... | collective-permute-start | bytes 442376 | tf_op jit(solution)/shard_map/ppermute | solution.py:269
  24.3 7.6 %collective-permute-start.7 = (bf16[2,9,32,128]{3,2,1,0:T(8,128)(2,1)S(1)}, bf16[2,9,32,128]{3,2,1,0:T(8,128)(2,1)S(1)}, u32[]{:S(2)}, u32[]{:S(2)}) collective-permute-start(bf16[2,9,32,128]{3,2,1,0:T(8,128)(2,1)S(1)} %collective-permute-done.1.refs_1_), channel_id=1, source_target_pairs={{0,12},{1,11},{2,14},{3,9},{4,8},{5,15},{6,10},{7,13},{8,4},{9,3},... | collective-permute-start | bytes 442376 | tf_op jit(solution)/shard_map/ppermute | solution.py:269
  25.8 6.4 %collective-permute-start.4 = (bf16[2,9,32,128]{3,2,1,0:T(8,128)(2,1)S(1)}, bf16[2,9,32,128]{3,2,1,0:T(8,128)(2,1)S(1)}, u32[]{:S(2)}, u32[]{:S(2)}) collective-permute-start(bf16[2,9,32,128]{3,2,1,0:T(8,128)(2,1)S(1)} %collective-permute-done.1.refs_1_), channel_id=1, source_target_pairs={{0,4},{1,9},{2,6},{3,11},{4,0},{5,13},{6,2},{7,15},{8,12},{9,1},{1... | collective-permute-start | bytes 442376 | tf_op jit(solution)/shard_map/ppermute | solution.py:269
  32.2 1.4 %collective-permute-start.9 = (bf16[2,9,32,128]{3,2,1,0:T(8,128)(2,1)S(1)}, bf16[2,9,32,128]{3,2,1,0:T(8,128)(2,1)S(1)}, u32[]{:S(2)}, u32[]{:S(2)}) collective-permute-start(bf16[2,9,32,128]{3,2,1,0:T(8,128)(2,1)S(1)} %collective-permute-done.4.refs_1_), channel_id=1, source_target_pairs={{0,1},{1,0},{2,3},{3,2},{4,5},{5,4},{6,7},{7,6},{8,9},{9,8},{10,11... | collective-permute-start | bytes 442376 | tf_op jit(solution)/shard_map/ppermute | solution.py:274
  32.4 1.5 %collective-permute-start.10 = (bf16[2,9,32,128]{3,2,1,0:T(8,128)(2,1)S(1)}, bf16[2,9,32,128]{3,2,1,0:T(8,128)(2,1)S(1)}, u32[]{:S(2)}, u32[]{:S(2)}) collective-permute-start(bf16[2,9,32,128]{3,2,1,0:T(8,128)(2,1)S(1)} %collective-permute-done.5.refs_2_), channel_id=1, source_target_pairs={{0,1},{1,0},{2,3},{3,2},{4,5},{5,4},{6,7},{7,6},{8,9},{9,8},{10,11... | collective-permute-start | bytes 442376 | tf_op jit(solution)/shard_map/ppermute | solution.py:274
  32.8 1.4 %collective-permute-start.11 = (bf16[2,9,32,128]{3,2,1,0:T(8,128)(2,1)S(1)}, bf16[2,9,32,128]{3,2,1,0:T(8,128)(2,1)S(1)}, u32[]{:S(2)}, u32[]{:S(2)}) collective-permute-start(bf16[2,9,32,128]{3,2,1,0:T(8,128)(2,1)S(1)} %collective-permute-done.6.refs_3_), channel_id=1, source_target_pairs={{0,1},{1,0},{2,3},{3,2},{4,5},{5,4},{6,7},{7,6},{8,9},{9,8},{10,11... | collective-permute-start | bytes 442376 | tf_op jit(solution)/shard_map/ppermute | solution.py:274
  32.9 1.5 %collective-permute-start.12 = (bf16[2,9,32,128]{3,2,1,0:T(8,128)(2,1)S(1)}, bf16[2,9,32,128]{3,2,1,0:T(8,128)(2,1)S(1)}, u32[]{:S(2)}, u32[]{:S(2)}) collective-permute-start(bf16[2,9,32,128]{3,2,1,0:T(8,128)(2,1)S(1)} %collective-permute-done.7.refs_4_), channel_id=1, source_target_pairs={{0,1},{1,0},{2,3},{3,2},{4,5},{5,4},{6,7},{7,6},{8,9},{9,8},{10,11... | collective-permute-start | bytes 442376 | tf_op jit(solution)/shard_map/ppermute | solution.py:274
  34.3 19.7 %copy-start.11 = (bf16[1,32,256]{2,1,0:T(8,128)(2,1)S(1)}, bf16[1,32,256]{2,1,0:T(8,128)(2,1)}, u32[]{:S(2)}) copy-start(bf16[1,32,256]{2,1,0:T(8,128)(2,1)} %get-tuple-element.153) | copy-start | bytes 49156
  37.8 23.4 %copy-start.10 = (bf16[1,32,256]{2,1,0:T(8,128)(2,1)S(1)}, bf16[1,32,256]{2,1,0:T(8,128)(2,1)}, u32[]{:S(2)}) copy-start(bf16[1,32,256]{2,1,0:T(8,128)(2,1)} %get-tuple-element.160) | copy-start | bytes 49156
  37.8 1.6 %collective-permute-start.13 = (bf16[2,2,9,32,128]{4,3,2,1,0:T(8,128)(2,1)S(1)}, bf16[2,2,9,32,128]{4,3,2,1,0:T(8,128)(2,1)S(1)}, u32[]{:S(2)}, u32[]{:S(2)}) collective-permute-start(bf16[2,2,9,32,128]{4,3,2,1,0:T(8,128)(2,1)S(1)} %get-tuple-element.127), channel_id=1, source_target_pairs={{0,1},{1,0},{2,3},{3,2},{4,5},{5,4},{6,7},{7,6},{8,9},{9,8},{10,11... | collective-permute-start | bytes 884744 | tf_op jit(solution)/shard_map/ppermute | solution.py:274
  39.5 11.1 %collective-permute-start.18 = (bf16[4,2,9,32,128]{4,3,2,1,0:T(8,128)(2,1)S(1)}, bf16[4,2,9,32,128]{4,3,2,1,0:T(8,128)(2,1)S(1)}, u32[]{:S(2)}, u32[]{:S(2)}) collective-permute-start(bf16[4,2,9,32,128]{4,3,2,1,0:T(8,128)(2,1)S(1)} %get-tuple-element.136), channel_id=1, source_target_pairs={{0,1},{1,0},{2,3},{3,2},{4,5},{5,4},{6,7},{7,6},{8,9},{9,8},{10,11... | collective-permute-start | bytes 1769480 | tf_op jit(solution)/shard_map/ppermute | solution.py:274
  39.9 2.3 %collective-permute-start.16 = (bf16[2,2,9,32,128]{4,3,2,1,0:T(8,128)(2,1)S(1)}, bf16[2,2,9,32,128]{4,3,2,1,0:T(8,128)(2,1)S(1)}, u32[]{:S(2)}, u32[]{:S(2)}) collective-permute-start(bf16[2,2,9,32,128]{4,3,2,1,0:T(8,128)(2,1)S(1)} %get-tuple-element.134), channel_id=1, source_target_pairs={{0,1},{1,0},{2,3},{3,2},{4,5},{5,4},{6,7},{7,6},{8,9},{9,8},{10,11... | collective-permute-start | bytes 884744 | tf_op jit(solution)/shard_map/ppermute | solution.py:274
  40.1 5.3 %collective-permute-start.14 = (bf16[2,9,32,128]{3,2,1,0:T(8,128)(2,1)S(1)}, bf16[2,9,32,128]{3,2,1,0:T(8,128)(2,1)S(1)}, u32[]{:S(2)}, u32[]{:S(2)}) collective-permute-start(bf16[2,9,32,128]{3,2,1,0:T(8,128)(2,1)S(1)} %get-tuple-element.131), channel_id=1, source_target_pairs={{0,4},{1,9},{2,6},{3,11},{4,0},{5,13},{6,2},{7,15},{8,12},{9,1},{1... | collective-permute-start | bytes 442376 | tf_op jit(solution)/shard_map/ppermute | solution.py:269
  41.1 5.1 %collective-permute-start.15 = (bf16[2,9,32,128]{3,2,1,0:T(8,128)(2,1)S(1)}, bf16[2,9,32,128]{3,2,1,0:T(8,128)(2,1)S(1)}, u32[]{:S(2)}, u32[]{:S(2)}) collective-permute-start(bf16[2,9,32,128]{3,2,1,0:T(8,128)(2,1)S(1)} %get-tuple-element.132), channel_id=1, source_target_pairs={{0,8},{1,3},{2,10},{3,1},{4,12},{5,7},{6,14},{7,5},{8,0},{9,11},{1... | collective-permute-start | bytes 442376 | tf_op jit(solution)/shard_map/ppermute | solution.py:269
  42.3 8.4 %collective-permute-start.17 = (bf16[2,9,32,128]{3,2,1,0:T(8,128)(2,1)S(1)}, bf16[2,9,32,128]{3,2,1,0:T(8,128)(2,1)S(1)}, u32[]{:S(2)}, u32[]{:S(2)}) collective-permute-start(bf16[2,9,32,128]{3,2,1,0:T(8,128)(2,1)S(1)} %get-tuple-element.135), channel_id=1, source_target_pairs={{0,2},{1,5},{2,0},{3,7},{4,6},{5,1},{6,4},{7,3},{8,10},{9,13},{10,... | collective-permute-start | bytes 442376 | tf_op jit(solution)/shard_map/ppermute | solution.py:269
  43.3 12.0 %collective-permute-start.22 = (bf16[2,9,32,128]{3,2,1,0:T(8,128)(2,1)S(1)}, bf16[2,9,32,128]{3,2,1,0:T(8,128)(2,1)S(1)}, u32[]{:S(2)}, u32[]{:S(2)}) collective-permute-start(bf16[2,9,32,128]{3,2,1,0:T(8,128)(2,1)S(1)} %get-tuple-element.151), channel_id=1, source_target_pairs={{0,14},{1,15},{2,12},{3,13},{4,10},{5,11},{6,8},{7,9},{8,6},{9,7},... | collective-permute-start | bytes 442376 | tf_op jit(solution)/shard_map/ppermute | solution.py:269
  50.8 8.8 %collective-permute-start.19 = (bf16[2,9,32,128]{3,2,1,0:T(8,128)(2,1)S(1)}, bf16[2,9,32,128]{3,2,1,0:T(8,128)(2,1)S(1)}, u32[]{:S(2)}, u32[]{:S(2)}) collective-permute-start(bf16[2,9,32,128]{3,2,1,0:T(8,128)(2,1)S(1)} %get-tuple-element.148), channel_id=1, source_target_pairs={{0,2},{1,5},{2,0},{3,7},{4,6},{5,1},{6,4},{7,3},{8,10},{9,13},{10,... | collective-permute-start | bytes 442376 | tf_op jit(solution)/shard_map/ppermute | solution.py:269
  51.9 7.8 %collective-permute-start.20 = (bf16[2,9,32,128]{3,2,1,0:T(8,128)(2,1)S(1)}, bf16[2,9,32,128]{3,2,1,0:T(8,128)(2,1)S(1)}, u32[]{:S(2)}, u32[]{:S(2)}) collective-permute-start(bf16[2,9,32,128]{3,2,1,0:T(8,128)(2,1)S(1)} %get-tuple-element.149), channel_id=1, source_target_pairs={{0,4},{1,9},{2,6},{3,11},{4,0},{5,13},{6,2},{7,15},{8,12},{9,1},{1... | collective-permute-start | bytes 442376 | tf_op jit(solution)/shard_map/ppermute | solution.py:269
  53.0 6.6 %collective-permute-start.21 = (bf16[2,9,32,128]{3,2,1,0:T(8,128)(2,1)S(1)}, bf16[2,9,32,128]{3,2,1,0:T(8,128)(2,1)S(1)}, u32[]{:S(2)}, u32[]{:S(2)}) collective-permute-start(bf16[2,9,32,128]{3,2,1,0:T(8,128)(2,1)S(1)} %get-tuple-element.150), channel_id=1, source_target_pairs={{0,8},{1,3},{2,10},{3,1},{4,12},{5,7},{6,14},{7,5},{8,0},{9,11},{1... | collective-permute-start | bytes 442376 | tf_op jit(solution)/shard_map/ppermute | solution.py:269
  54.0 5.6 %collective-permute-start.23 = (bf16[1,32,256]{2,1,0:T(8,128)(2,1)S(1)}, bf16[1,32,256]{2,1,0:T(8,128)(2,1)S(1)}, u32[]{:S(2)}, u32[]{:S(2)}) collective-permute-start(bf16[1,32,256]{2,1,0:T(8,128)(2,1)S(1)} %copy-done.11), channel_id=1, source_target_pairs={{1,3},{3,5},{5,7},{7,9},{9,11},{11,13},{13,15},{15,17},{17,19},{19... | collective-permute-start | bytes 49160 | tf_op jit(solution)/shard_map/ppermute | solution.py:435
  59.8 6.1 %collective-permute-start.24 = (bf16[9,32,128]{2,1,0:T(8,128)(2,1)S(1)}, bf16[9,32,128]{2,1,0:T(8,128)(2,1)S(1)}, u32[]{:S(2)}, u32[]{:S(2)}) collective-permute-start(bf16[9,32,128]{2,1,0:T(8,128)(2,1)S(1)} %get-tuple-element.159), channel_id=1, source_target_pairs={{0,16},{1,17},{2,18},{3,19},{4,20},{5,21},{6,22},{7,23},{8,24},{9,... | collective-permute-start | bytes 221192 | tf_op jit(solution)/shard_map/ppermute | solution.py:265
  61.2 1.2 collective-permute-start.25
  61.2 1.3 %collective-permute-start.26 = (bf16[1,32,256]{2,1,0:T(8,128)(2,1)S(1)}, bf16[1,32,256]{2,1,0:T(8,128)(2,1)S(1)}, u32[]{:S(2)}, u32[]{:S(2)}) collective-permute-start(bf16[1,32,256]{2,1,0:T(8,128)(2,1)S(1)} %collective-permute-done.23), channel_id=1, source_target_pairs={{0,1},{1,0},{2,3},{3,2},{4,5},{5,4},{6,7},{7,6},{8,9},{9,8},{10,11... | collective-permute-start | bytes 49160 | tf_op jit(solution)/shard_map/ppermute | solution.py:274
  67.5 5.8 %collective-permute-start.27 = (bf16[9,32,128]{2,1,0:T(8,128)(2,1)S(1)}, bf16[9,32,128]{2,1,0:T(8,128)(2,1)S(1)}, u32[]{:S(2)}, u32[]{:S(2)}) collective-permute-start(bf16[9,32,128]{2,1,0:T(8,128)(2,1)S(1)} %get-tuple-element.166.refs_0_), channel_id=1, source_target_pairs={{0,16},{1,17},{2,18},{3,19},{4,20},{5,21},{6,22},{7,23},{8,24},{9,... | collective-permute-start | bytes 221192 | tf_op jit(solution)/shard_map/ppermute | solution.py:265
  73.3 6.8 %collective-permute-start.30 = (bf16[2,9,32,128]{3,2,1,0:T(8,128)(2,1)S(1)}, bf16[2,9,32,128]{3,2,1,0:T(8,128)(2,1)S(1)}, u32[]{:S(2)}, u32[]{:S(2)}) collective-permute-start(bf16[2,9,32,128]{3,2,1,0:T(8,128)(2,1)S(1)} %shard_map.108.refs_0_), channel_id=1, source_target_pairs={{0,8},{1,3},{2,10},{3,1},{4,12},{5,7},{6,14},{7,5},{8,0},{9,11},{1... | collective-permute-start | bytes 442376 | tf_op jit(solution)/shard_map/ppermute | solution.py:269
  73.4 6.8 %collective-permute-start.29 = (bf16[2,9,32,128]{3,2,1,0:T(8,128)(2,1)S(1)}, bf16[2,9,32,128]{3,2,1,0:T(8,128)(2,1)S(1)}, u32[]{:S(2)}, u32[]{:S(2)}) collective-permute-start(bf16[2,9,32,128]{3,2,1,0:T(8,128)(2,1)S(1)} %shard_map.108.refs_0_), channel_id=1, source_target_pairs={{0,4},{1,9},{2,6},{3,11},{4,0},{5,13},{6,2},{7,15},{8,12},{9,1},{1... | collective-permute-start | bytes 442376 | tf_op jit(solution)/shard_map/ppermute | solution.py:269
  74.3 7.2 %collective-permute-start.28 = (bf16[2,9,32,128]{3,2,1,0:T(8,128)(2,1)S(1)}, bf16[2,9,32,128]{3,2,1,0:T(8,128)(2,1)S(1)}, u32[]{:S(2)}, u32[]{:S(2)}) collective-permute-start(bf16[2,9,32,128]{3,2,1,0:T(8,128)(2,1)S(1)} %shard_map.108.refs_0_), channel_id=1, source_target_pairs={{0,2},{1,5},{2,0},{3,7},{4,6},{5,1},{6,4},{7,3},{8,10},{9,13},{10,... | collective-permute-start | bytes 442376 | tf_op jit(solution)/shard_map/ppermute | solution.py:269
  77.7 11.2 %collective-permute-start.34 = (bf16[2,9,32,128]{3,2,1,0:T(8,128)(2,1)S(1)}, bf16[2,9,32,128]{3,2,1,0:T(8,128)(2,1)S(1)}, u32[]{:S(2)}, u32[]{:S(2)}) collective-permute-start(bf16[2,9,32,128]{3,2,1,0:T(8,128)(2,1)S(1)} %shard_map.108.refs_0_), channel_id=1, source_target_pairs={{0,14},{1,15},{2,12},{3,13},{4,10},{5,11},{6,8},{7,9},{8,6},{9,7},... | collective-permute-start | bytes 442376 | tf_op jit(solution)/shard_map/ppermute | solution.py:269
  81.6 7.9 %collective-permute-start.31 = (bf16[2,9,32,128]{3,2,1,0:T(8,128)(2,1)S(1)}, bf16[2,9,32,128]{3,2,1,0:T(8,128)(2,1)S(1)}, u32[]{:S(2)}, u32[]{:S(2)}) collective-permute-start(bf16[2,9,32,128]{3,2,1,0:T(8,128)(2,1)S(1)} %collective-permute-done.28.refs_1_), channel_id=1, source_target_pairs={{0,4},{1,9},{2,6},{3,11},{4,0},{5,13},{6,2},{7,15},{8,12},{9,1},{1... | collective-permute-start | bytes 442376 | tf_op jit(solution)/shard_map/ppermute | solution.py:269
  81.6 7.3 %collective-permute-start.35 = (bf16[1,32,256]{2,1,0:T(8,128)(2,1)S(1)}, bf16[1,32,256]{2,1,0:T(8,128)(2,1)S(1)}, u32[]{:S(2)}, u32[]{:S(2)}) collective-permute-start(bf16[1,32,256]{2,1,0:T(8,128)(2,1)S(1)} %get-tuple-element.173), channel_id=1, source_target_pairs={{1,3},{3,5},{5,7},{7,9},{9,11},{11,13},{13,15},{15,17},{17,19},{19... | collective-permute-start | bytes 49160 | tf_op jit(solution)/shard_map/ppermute | solution.py:417
  82.9 9.3 %collective-permute-start.33 = (bf16[2,9,32,128]{3,2,1,0:T(8,128)(2,1)S(1)}, bf16[2,9,32,128]{3,2,1,0:T(8,128)(2,1)S(1)}, u32[]{:S(2)}, u32[]{:S(2)}) collective-permute-start(bf16[2,9,32,128]{3,2,1,0:T(8,128)(2,1)S(1)} %collective-permute-done.29.refs_2_), channel_id=1, source_target_pairs={{0,8},{1,3},{2,10},{3,1},{4,12},{5,7},{6,14},{7,5},{8,0},{9,11},{1... | collective-permute-start | bytes 442376 | tf_op jit(solution)/shard_map/ppermute | solution.py:269
  88.9 5.1 %collective-permute-start.32 = (bf16[2,9,32,128]{3,2,1,0:T(8,128)(2,1)S(1)}, bf16[2,9,32,128]{3,2,1,0:T(8,128)(2,1)S(1)}, u32[]{:S(2)}, u32[]{:S(2)}) collective-permute-start(bf16[2,9,32,128]{3,2,1,0:T(8,128)(2,1)S(1)} %collective-permute-done.30.refs_4_), channel_id=1, source_target_pairs={{0,2},{1,5},{2,0},{3,7},{4,6},{5,1},{6,4},{7,3},{8,10},{9,13},{10,... | collective-permute-start | bytes 442376 | tf_op jit(solution)/shard_map/ppermute | solution.py:269
  88.9 5.1 %collective-permute-start.36 = (bf16[2,9,32,128]{3,2,1,0:T(8,128)(2,1)S(1)}, bf16[2,9,32,128]{3,2,1,0:T(8,128)(2,1)S(1)}, u32[]{:S(2)}, u32[]{:S(2)}) collective-permute-start(bf16[2,9,32,128]{3,2,1,0:T(8,128)(2,1)S(1)} %shard_map.108.refs_0_), channel_id=1, source_target_pairs={{0,1},{1,0},{2,3},{3,2},{4,5},{5,4},{6,7},{7,6},{8,9},{9,8},{10,11... | collective-permute-start | bytes 442376 | tf_op jit(solution)/shard_map/ppermute | solution.py:274
  88.9 5.6 %collective-permute-start.37 = (bf16[2,9,32,128]{3,2,1,0:T(8,128)(2,1)S(1)}, bf16[2,9,32,128]{3,2,1,0:T(8,128)(2,1)S(1)}, u32[]{:S(2)}, u32[]{:S(2)}) collective-permute-start(bf16[2,9,32,128]{3,2,1,0:T(8,128)(2,1)S(1)} %collective-permute-done.28.refs_1_), channel_id=1, source_target_pairs={{0,1},{1,0},{2,3},{3,2},{4,5},{5,4},{6,7},{7,6},{8,9},{9,8},{10,11... | collective-permute-start | bytes 442376 | tf_op jit(solution)/shard_map/ppermute | solution.py:274
  89.4 5.2 %collective-permute-start.38 = (bf16[2,9,32,128]{3,2,1,0:T(8,128)(2,1)S(1)}, bf16[2,9,32,128]{3,2,1,0:T(8,128)(2,1)S(1)}, u32[]{:S(2)}, u32[]{:S(2)}) collective-permute-start(bf16[2,9,32,128]{3,2,1,0:T(8,128)(2,1)S(1)} %collective-permute-done.29.refs_2_), channel_id=1, source_target_pairs={{0,1},{1,0},{2,3},{3,2},{4,5},{5,4},{6,7},{7,6},{8,9},{9,8},{10,11... | collective-permute-start | bytes 442376 | tf_op jit(solution)/shard_map/ppermute | solution.py:274
  92.1 3.0 %collective-permute-start.40 = (bf16[2,9,32,128]{3,2,1,0:T(8,128)(2,1)S(1)}, bf16[2,9,32,128]{3,2,1,0:T(8,128)(2,1)S(1)}, u32[]{:S(2)}, u32[]{:S(2)}) collective-permute-start(bf16[2,9,32,128]{3,2,1,0:T(8,128)(2,1)S(1)} %collective-permute-done.30.refs_4_), channel_id=1, source_target_pairs={{0,1},{1,0},{2,3},{3,2},{4,5},{5,4},{6,7},{7,6},{8,9},{9,8},{10,11... | collective-permute-start | bytes 442376 | tf_op jit(solution)/shard_map/ppermute | solution.py:274
  94.0 1.4 %collective-permute-start.39 = (bf16[2,9,32,128]{3,2,1,0:T(8,128)(2,1)S(1)}, bf16[2,9,32,128]{3,2,1,0:T(8,128)(2,1)S(1)}, u32[]{:S(2)}, u32[]{:S(2)}) collective-permute-start(bf16[2,9,32,128]{3,2,1,0:T(8,128)(2,1)S(1)} %collective-permute-done.31.refs_3_), channel_id=1, source_target_pairs={{0,1},{1,0},{2,3},{3,2},{4,5},{5,4},{6,7},{7,6},{8,9},{9,8},{10,11... | collective-permute-start | bytes 442376 | tf_op jit(solution)/shard_map/ppermute | solution.py:274
  94.1 1.6 %collective-permute-start.41 = (bf16[2,9,32,128]{3,2,1,0:T(8,128)(2,1)S(1)}, bf16[2,9,32,128]{3,2,1,0:T(8,128)(2,1)S(1)}, u32[]{:S(2)}, u32[]{:S(2)}) collective-permute-start(bf16[2,9,32,128]{3,2,1,0:T(8,128)(2,1)S(1)} %collective-permute-done.32.refs_5_), channel_id=1, source_target_pairs={{0,1},{1,0},{2,3},{3,2},{4,5},{5,4},{6,7},{7,6},{8,9},{9,8},{10,11... | collective-permute-start | bytes 442376 | tf_op jit(solution)/shard_map/ppermute | solution.py:274
  94.6 1.4 %collective-permute-start.42 = (bf16[2,9,32,128]{3,2,1,0:T(8,128)(2,1)S(1)}, bf16[2,9,32,128]{3,2,1,0:T(8,128)(2,1)S(1)}, u32[]{:S(2)}, u32[]{:S(2)}) collective-permute-start(bf16[2,9,32,128]{3,2,1,0:T(8,128)(2,1)S(1)} %collective-permute-done.33.refs_6_), channel_id=1, source_target_pairs={{0,1},{1,0},{2,3},{3,2},{4,5},{5,4},{6,7},{7,6},{8,9},{9,8},{10,11... | collective-permute-start | bytes 442376 | tf_op jit(solution)/shard_map/ppermute | solution.py:274
  94.6 1.5 %collective-permute-start.43 = (bf16[2,9,32,128]{3,2,1,0:T(8,128)(2,1)S(1)}, bf16[2,9,32,128]{3,2,1,0:T(8,128)(2,1)S(1)}, u32[]{:S(2)}, u32[]{:S(2)}) collective-permute-start(bf16[2,9,32,128]{3,2,1,0:T(8,128)(2,1)S(1)} %collective-permute-done.34.refs_7_), channel_id=1, source_target_pairs={{0,1},{1,0},{2,3},{3,2},{4,5},{5,4},{6,7},{7,6},{8,9},{9,8},{10,11... | collective-permute-start | bytes 442376 | tf_op jit(solution)/shard_map/ppermute | solution.py:274
  99.6 1.6 %collective-permute-start.44 = (bf16[2,2,9,32,128]{4,3,2,1,0:T(8,128)(2,1)S(1)}, bf16[2,2,9,32,128]{4,3,2,1,0:T(8,128)(2,1)S(1)}, u32[]{:S(2)}, u32[]{:S(2)}) collective-permute-start(bf16[2,2,9,32,128]{4,3,2,1,0:T(8,128)(2,1)S(1)} %get-tuple-element.184), channel_id=1, source_target_pairs={{0,1},{1,0},{2,3},{3,2},{4,5},{5,4},{6,7},{7,6},{8,9},{9,8},{10,11... | collective-permute-start | bytes 884744 | tf_op jit(solution)/shard_map/ppermute | solution.py:274
  101.3 10.3 %collective-permute-start.50 = (bf16[4,2,9,32,128]{4,3,2,1,0:T(8,128)(2,1)S(1)}, bf16[4,2,9,32,128]{4,3,2,1,0:T(8,128)(2,1)S(1)}, u32[]{:S(2)}, u32[]{:S(2)}) collective-permute-start(bf16[4,2,9,32,128]{4,3,2,1,0:T(8,128)(2,1)S(1)} %get-tuple-element.194), channel_id=1, source_target_pairs={{0,1},{1,0},{2,3},{3,2},{4,5},{5,4},{6,7},{7,6},{8,9},{9,8},{10,11... | collective-permute-start | bytes 1769480 | tf_op jit(solution)/shard_map/ppermute | solution.py:274
  101.7 2.1 %collective-permute-start.47 = (bf16[2,2,9,32,128]{4,3,2,1,0:T(8,128)(2,1)S(1)}, bf16[2,2,9,32,128]{4,3,2,1,0:T(8,128)(2,1)S(1)}, u32[]{:S(2)}, u32[]{:S(2)}) collective-permute-start(bf16[2,2,9,32,128]{4,3,2,1,0:T(8,128)(2,1)S(1)} %get-tuple-element.191), channel_id=1, source_target_pairs={{0,1},{1,0},{2,3},{3,2},{4,5},{5,4},{6,7},{7,6},{8,9},{9,8},{10,11... | collective-permute-start | bytes 884744 | tf_op jit(solution)/shard_map/ppermute | solution.py:274
  101.9 5.3 %collective-permute-start.45 = (bf16[2,9,32,128]{3,2,1,0:T(8,128)(2,1)S(1)}, bf16[2,9,32,128]{3,2,1,0:T(8,128)(2,1)S(1)}, u32[]{:S(2)}, u32[]{:S(2)}) collective-permute-start(bf16[2,9,32,128]{3,2,1,0:T(8,128)(2,1)S(1)} %get-tuple-element.188), channel_id=1, source_target_pairs={{0,4},{1,9},{2,6},{3,11},{4,0},{5,13},{6,2},{7,15},{8,12},{9,1},{1... | collective-permute-start | bytes 442376 | tf_op jit(solution)/shard_map/ppermute | solution.py:269
  101.9 6.7 %collective-permute-start.46 = (bf16[2,9,32,128]{3,2,1,0:T(8,128)(2,1)S(1)}, bf16[2,9,32,128]{3,2,1,0:T(8,128)(2,1)S(1)}, u32[]{:S(2)}, u32[]{:S(2)}) collective-permute-start(bf16[2,9,32,128]{3,2,1,0:T(8,128)(2,1)S(1)} %get-tuple-element.189), channel_id=1, source_target_pairs={{0,8},{1,3},{2,10},{3,1},{4,12},{5,7},{6,14},{7,5},{8,0},{9,11},{1... | collective-permute-start | bytes 442376 | tf_op jit(solution)/shard_map/ppermute | solution.py:269
  103.9 6.8 %collective-permute-start.48 = (bf16[2,9,32,128]{3,2,1,0:T(8,128)(2,1)S(1)}, bf16[2,9,32,128]{3,2,1,0:T(8,128)(2,1)S(1)}, u32[]{:S(2)}, u32[]{:S(2)}) collective-permute-start(bf16[2,9,32,128]{3,2,1,0:T(8,128)(2,1)S(1)} %get-tuple-element.192), channel_id=1, source_target_pairs={{0,2},{1,5},{2,0},{3,7},{4,6},{5,1},{6,4},{7,3},{8,10},{9,13},{10,... | collective-permute-start | bytes 442376 | tf_op jit(solution)/shard_map/ppermute | solution.py:269
  104.0 7.7 %collective-permute-start.49 = (bf16[2,9,32,128]{3,2,1,0:T(8,128)(2,1)S(1)}, bf16[2,9,32,128]{3,2,1,0:T(8,128)(2,1)S(1)}, u32[]{:S(2)}, u32[]{:S(2)}) collective-permute-start(bf16[2,9,32,128]{3,2,1,0:T(8,128)(2,1)S(1)} %get-tuple-element.193), channel_id=1, source_target_pairs={{0,12},{1,11},{2,14},{3,9},{4,8},{5,15},{6,10},{7,13},{8,4},{9,3},... | collective-permute-start | bytes 442376 | tf_op jit(solution)/shard_map/ppermute | solution.py:269
  111.9 6.1 %collective-permute-start.51 = (bf16[2,9,32,128]{3,2,1,0:T(8,128)(2,1)S(1)}, bf16[2,9,32,128]{3,2,1,0:T(8,128)(2,1)S(1)}, u32[]{:S(2)}, u32[]{:S(2)}) collective-permute-start(bf16[2,9,32,128]{3,2,1,0:T(8,128)(2,1)S(1)} %get-tuple-element.207), channel_id=1, source_target_pairs={{0,2},{1,5},{2,0},{3,7},{4,6},{5,1},{6,4},{7,3},{8,10},{9,13},{10,... | collective-permute-start | bytes 442376 | tf_op jit(solution)/shard_map/ppermute | solution.py:269
  113.0 5.1 %collective-permute-start.52 = (bf16[2,9,32,128]{3,2,1,0:T(8,128)(2,1)S(1)}, bf16[2,9,32,128]{3,2,1,0:T(8,128)(2,1)S(1)}, u32[]{:S(2)}, u32[]{:S(2)}) collective-permute-start(bf16[2,9,32,128]{3,2,1,0:T(8,128)(2,1)S(1)} %get-tuple-element.208), channel_id=1, source_target_pairs={{0,4},{1,9},{2,6},{3,11},{4,0},{5,13},{6,2},{7,15},{8,12},{9,1},{1... | collective-permute-start | bytes 442376 | tf_op jit(solution)/shard_map/ppermute | solution.py:269
  113.4 5.1 %collective-permute-start.53 = (bf16[2,9,32,128]{3,2,1,0:T(8,128)(2,1)S(1)}, bf16[2,9,32,128]{3,2,1,0:T(8,128)(2,1)S(1)}, u32[]{:S(2)}, u32[]{:S(2)}) collective-permute-start(bf16[2,9,32,128]{3,2,1,0:T(8,128)(2,1)S(1)} %get-tuple-element.209), channel_id=1, source_target_pairs={{0,8},{1,3},{2,10},{3,1},{4,12},{5,7},{6,14},{7,5},{8,0},{9,11},{1... | collective-permute-start | bytes 442376 | tf_op jit(solution)/shard_map/ppermute | solution.py:269
  118.6 6.2 %collective-permute-start.54 = (bf16[9,32,128]{2,1,0:T(8,128)(2,1)S(1)}, bf16[9,32,128]{2,1,0:T(8,128)(2,1)S(1)}, u32[]{:S(2)}, u32[]{:S(2)}) collective-permute-start(bf16[9,32,128]{2,1,0:T(8,128)(2,1)S(1)} %get-tuple-element.216), channel_id=1, source_target_pairs={{0,16},{1,17},{2,18},{3,19},{4,20},{5,21},{6,22},{7,23},{8,24},{9,... | collective-permute-start | bytes 221192 | tf_op jit(solution)/shard_map/ppermute | solution.py:265
  118.7 1.2 collective-permute-start.55
  118.7 1.3 %collective-permute-start.56 = (bf16[1,32,256]{2,1,0:T(8,128)(2,1)S(1)}, bf16[1,32,256]{2,1,0:T(8,128)(2,1)S(1)}, u32[]{:S(2)}, u32[]{:S(2)}) collective-permute-start(bf16[1,32,256]{2,1,0:T(8,128)(2,1)S(1)} %collective-permute-done.35), channel_id=1, source_target_pairs={{0,1},{1,0},{2,3},{3,2},{4,5},{5,4},{6,7},{7,6},{8,9},{9,8},{10,11... | collective-permute-start | bytes 49160 | tf_op jit(solution)/shard_map/ppermute | solution.py:274
  (5 other events, 28.7 us)

commit v24 on v22

--- a/solution.py
+++ b/solution.py
@@ -398,6 +398,8 @@
 
     def apply_matrix(field_in, coeffs, inner, outer, coupling, with_coeffs):
         away = [swap_far(coeffs, s) for s in range(1, far)]
+        if not with_coeffs:
+            away, outer = barrier((away, lax.ppermute(outer, "clu", halo_pairs)))
         (column,) = first_join(relaid(coupling, coeffs), coeffs, *away) if with_coeffs else join(coeffs, *away)
         got = {0: column, x: swap(column, x), y: swap(column, y), z: swap(column, z)}
         near_sum = near(field_in, near_field)
@@ -413,7 +415,7 @@
             corner = swap(column, x | y | z)
             other = {chip: swap_cores(part) for chip, part in got.items()}
             got |= second_round
-            got, corner, outer = barrier((got, corner, lax.ppermute(outer, "clu", halo_pairs)))
+            got, corner = barrier((got, corner))
             got[x | y | z] = corner
             other |= {chip: swap_cores(got[chip]) for chip in order[0]}
             args = [got[chip] for chip in range(chips)] + [other[chip] for chip in range(chips)]

time: 125 us -> 127 us (1.016)
  starting transfers between devices: 53 us -> 54.9 us
    ppermute x1, waiting for transfers between devices: 0.01 us -> 4.62 us  [apply_matrix(): away, outer = barrier((away, lax.ppermute(outer, 'clu', halo_pairs)))]
    ppermute x4, waiting for transfers between devices: 10.3 us -> 6.34 us  [swap_far(): lax.ppermute(part, 'clu', [(d, (d + shift * cube) % devices) for d in ran...]
    ppermute x28, starting transfers between devices: 37 us -> 39.9 us  [swap(): lax.ppermute(part, 'clu', [(d, d ^ (turned if d % cores else direction) *...]
  transfers between devices with their start and end apart: 55 -> 55, of which waited for: 39 -> 38; matrix products, arithmetic and copies ran while one was open for 4% -> 4% of each run, Pallas kernels for 2% -> 2%
where the time goes in v24:
time: 127 us
  starting transfers between devices  54.9 us (43%)
  waiting for transfers between devices  49.7 us (39%)
  Pallas kernels  16 us (13%)
  local copies, waits for them, and re-layouts  5.66 us (4%)
    ppermute x28, starting transfers between devices, swap(): lax.ppermute(part, 'clu', [(d, d ^ (turned if d % cores else direction) *...  39.9 us
    ppermute x28, waiting for transfers between devices, swap(): lax.ppermute(part, 'clu', [(d, d ^ (turned if d % cores else direction) *...  26.9 us
    ppermute x21, waiting for transfers between devices, swap_cores(): return lax.ppermute(part, 'clu', [(d, d ^ 1) for d in range(devices)])  7.58 us
    ppermute x4, starting transfers between devices, swap_far(): lax.ppermute(part, 'clu', [(d, (d + shift * cube) % devices) for d in ran...  7.4 us
    pallas_call x2, Pallas kernels, couple(): pl.pallas_call(functools.partial(couple_kernel, order=order, joined=joine...  6.93 us
    ppermute x4, waiting for transfers between devices, swap_far(): lax.ppermute(part, 'clu', [(d, (d + shift * cube) % devices) for d in ran...  6.34 us
    unnamed x25, local copies, waits for them, and re-layouts  5.66 us
    ppermute x21, starting transfers between devices, swap_cores(): return lax.ppermute(part, 'clu', [(d, d ^ 1) for d in range(devices)])  5 us
  transfers between devices with their start and end apart: 55, of which 38 were waited for; matrix products, arithmetic and copies ran while one was open for 4% of the time, Pallas kernels for 2%

profile of v24, /device:TPU:0, one launch (start us, length us, event | category | flops | bytes accessed | tf_op | source)
XLA Modules:
  0.0 127.1 jit_solution(5989043989553563144)
XLA Ops:
  0.6 2.9 %shard_map.95 = (bf16[9,32,128]{2,1,0:T(8,128)(2,1)}, bf16[1,32,256]{2,1,0:T(8,128)(2,1)}, bf16[1,32,256]{2,1,0:T(8,128)(2,1)}) custom-call(s32[12]{0:T(128)} %ranks_ref.5, bf16[8,32,256]{2,1,0:T(8,128)(2,1)} %v_ref.1, bf16[8,96,256]{2,1,0:T(8,128)(2,1)} %basis_ref.3, bf16[8,96,96]{2,1,0:T(8,128)(2,1)} %transfer_ref.3), custom_call_target="tpu_custom_call" | custom-call | tf_op jit(solution)/shard_map/pallas_call | solution.py:297
  3.6 4.1 %collective-permute-start = (bf16[9,32,128]{2,1,0:T(8,128)(2,1)}, bf16[9,32,128]{2,1,0:T(8,128)(2,1)S(1)}, u32[]{:S(2)}, u32[]{:S(2)}) collective-permute-start(bf16[9,32,128]{2,1,0:T(8,128)(2,1)} %get-tuple-element.113.__.refs_0_), channel_id=1, source_target_pairs={{0,16},{1,17},{2,18},{3,19},{4,20},{5,21},{6,22},{7,23},{8,24},{9,... | collective-permute-start | bytes 221192 | tf_op jit(solution)/shard_map/ppermute | solution.py:265
  7.7 4.8 %copy.10._.coupling_ref = bf16[128,96,96]{2,1,0:T(8,128)(2,1)} copy(bf16[128,96,96]{0,2,1:T(8,128)(2,1)} %param.12) | data formatting | bytes 4718592 | tf_op args[4]
  12.5 0.6 shard_map.96._
  13.0 0.8 copy-done.6
  13.9 1.6 %collective-permute-start.3 = (bf16[2,9,32,128]{3,2,1,0:T(8,128)(2,1)S(1)}, bf16[2,9,32,128]{3,2,1,0:T(8,128)(2,1)S(1)}, u32[]{:S(2)}, u32[]{:S(2)}) collective-permute-start(bf16[2,9,32,128]{3,2,1,0:T(8,128)(2,1)S(1)} %shard_map.97.refs_0_), channel_id=1, source_target_pairs={{0,8},{1,3},{2,10},{3,1},{4,12},{5,7},{6,14},{7,5},{8,0},{9,11},{1... | collective-permute-start | bytes 442376 | tf_op jit(solution)/shard_map/ppermute | solution.py:269
  15.5 1.5 %collective-permute-start.2 = (bf16[2,9,32,128]{3,2,1,0:T(8,128)(2,1)S(1)}, bf16[2,9,32,128]{3,2,1,0:T(8,128)(2,1)S(1)}, u32[]{:S(2)}, u32[]{:S(2)}) collective-permute-start(bf16[2,9,32,128]{3,2,1,0:T(8,128)(2,1)S(1)} %shard_map.97.refs_0_), channel_id=1, source_target_pairs={{0,4},{1,9},{2,6},{3,11},{4,0},{5,13},{6,2},{7,15},{8,12},{9,1},{1... | collective-permute-start | bytes 442376 | tf_op jit(solution)/shard_map/ppermute | solution.py:269
  17.0 1.5 %collective-permute-start.1 = (bf16[2,9,32,128]{3,2,1,0:T(8,128)(2,1)S(1)}, bf16[2,9,32,128]{3,2,1,0:T(8,128)(2,1)S(1)}, u32[]{:S(2)}, u32[]{:S(2)}) collective-permute-start(bf16[2,9,32,128]{3,2,1,0:T(8,128)(2,1)S(1)} %shard_map.97.refs_0_), channel_id=1, source_target_pairs={{0,2},{1,5},{2,0},{3,7},{4,6},{5,1},{6,4},{7,3},{8,10},{9,13},{10,... | collective-permute-start | bytes 442376 | tf_op jit(solution)/shard_map/ppermute | solution.py:269
  18.5 0.6 shard_map.98.near_ref
  19.1 1.3 %collective-permute-done.3.refs_3_ = bf16[2,9,32,128]{3,2,1,0:T(8,128)(2,1)S(1)} collective-permute-done((bf16[2,9,32,128]{3,2,1,0:T(8,128)(2,1)S(1)}, bf16[2,9,32,128]{3,2,1,0:T(8,128)(2,1)S(1)}, u32[]{:S(2)}, u32[]{:S(2)}) %collective-permute-start.3) | collective-permute-done | bytes 147488 | tf_op jit(solution)/shard_map/ppermute | solution.py:269
  20.5 1.3 %collective-permute-done.2.refs_2_ = bf16[2,9,32,128]{3,2,1,0:T(8,128)(2,1)S(1)} collective-permute-done((bf16[2,9,32,128]{3,2,1,0:T(8,128)(2,1)S(1)}, bf16[2,9,32,128]{3,2,1,0:T(8,128)(2,1)S(1)}, u32[]{:S(2)}, u32[]{:S(2)}) %collective-permute-start.2) | collective-permute-done | bytes 147488 | tf_op jit(solution)/shard_map/ppermute | solution.py:269
  22.3 0.5 collective-permute-start.6
  22.8 1.5 %collective-permute-start.7 = (bf16[2,9,32,128]{3,2,1,0:T(8,128)(2,1)S(1)}, bf16[2,9,32,128]{3,2,1,0:T(8,128)(2,1)S(1)}, u32[]{:S(2)}, u32[]{:S(2)}) collective-permute-start(bf16[2,9,32,128]{3,2,1,0:T(8,128)(2,1)S(1)} %collective-permute-done.3.refs_3_), channel_id=1, source_target_pairs={{0,2},{1,5},{2,0},{3,7},{4,6},{5,1},{6,4},{7,3},{8,10},{9,13},{10,... | collective-permute-start | bytes 442376 | tf_op jit(solution)/shard_map/ppermute | solution.py:269
  24.8 2.5 %collective-permute-start.4 = (bf16[2,9,32,128]{3,2,1,0:T(8,128)(2,1)S(1)}, bf16[2,9,32,128]{3,2,1,0:T(8,128)(2,1)S(1)}, u32[]{:S(2)}, u32[]{:S(2)}) collective-permute-start(bf16[2,9,32,128]{3,2,1,0:T(8,128)(2,1)S(1)} %collective-permute-done.1.refs_1_), channel_id=1, source_target_pairs={{0,12},{1,11},{2,14},{3,9},{4,8},{5,15},{6,10},{7,13},{8,4},{9,3},... | collective-permute-start | bytes 442376 | tf_op jit(solution)/shard_map/ppermute | solution.py:269
  27.3 0.9 collective-permute-done.6.refs_3_
  28.6 1.6 %collective-permute-done.5.refs_2_ = bf16[2,9,32,128]{3,2,1,0:T(8,128)(2,1)S(1)} collective-permute-done((bf16[2,9,32,128]{3,2,1,0:T(8,128)(2,1)S(1)}, bf16[2,9,32,128]{3,2,1,0:T(8,128)(2,1)S(1)}, u32[]{:S(2)}, u32[]{:S(2)}) %collective-permute-start.5) | collective-permute-done | bytes 147488 | tf_op jit(solution)/shard_map/ppermute | solution.py:269
  30.2 2.3 %collective-permute-done.4.refs_1_ = bf16[2,9,32,128]{3,2,1,0:T(8,128)(2,1)S(1)} collective-permute-done((bf16[2,9,32,128]{3,2,1,0:T(8,128)(2,1)S(1)}, bf16[2,9,32,128]{3,2,1,0:T(8,128)(2,1)S(1)}, u32[]{:S(2)}, u32[]{:S(2)}) %collective-permute-start.4) | collective-permute-done | bytes 147488 | tf_op jit(solution)/shard_map/ppermute | solution.py:269
  34.9 3.5 %shard_map.101 = (bf16[4,2,9,32,128]{4,3,2,1,0:T(8,128)(2,1)S(1)}, bf16[4,2,9,32,128]{4,3,2,1,0:T(8,128)(2,1)S(1)}, bf16[4,2,9,32,128]{4,3,2,1,0:T(8,128)(2,1)S(1)}, bf16[4,2,9,32,128]{4,3,2,1,0:T(8,128)(2,1)S(1)}) custom-call(s32[128]{0:T(128)S(1)} %bitcast.4, s32[128]{0:T(128)S(1)} %bitcast.6, bf16[128,96,96]{2,1,0:T(8,128)(2,1)S(1)} %copy-done.1, ...), custom_call_target="tpu_custom_call" | custom-call | flops 75497472 | bytes 10485760 | tf_op jit(solution)/shard_map/pallas_call | solution.py:312
  38.7 1.8 %collective-permute-done.13.swap_ref = bf16[4,2,9,32,128]{4,3,2,1,0:T(8,128)(2,1)S(1)} collective-permute-done((bf16[4,2,9,32,128]{4,3,2,1,0:T(8,128)(2,1)S(1)}, bf16[4,2,9,32,128]{4,3,2,1,0:T(8,128)(2,1)S(1)}, u32[]{:S(2)}, u32[]{:S(2)}) %collective-permute-start.13) | collective-permute-done | bytes 589856 | tf_op jit(solution)/shard_map/ppermute | solution.py:274
  40.9 1.0 collective-permute-start.14
  42.3 1.5 %collective-permute-start.16 = (bf16[2,9,32,128]{3,2,1,0:T(8,128)(2,1)S(1)}, bf16[2,9,32,128]{3,2,1,0:T(8,128)(2,1)S(1)}, u32[]{:S(2)}, u32[]{:S(2)}) collective-permute-start(bf16[2,9,32,128]{3,2,1,0:T(8,128)(2,1)S(1)} %get-tuple-element.136), channel_id=1, source_target_pairs={{0,2},{1,5},{2,0},{3,7},{4,6},{5,1},{6,4},{7,3},{8,10},{9,13},{10,... | collective-permute-start | bytes 442376 | tf_op jit(solution)/shard_map/ppermute | solution.py:269
  43.8 2.0 %collective-permute-start.21 = (bf16[2,9,32,128]{3,2,1,0:T(8,128)(2,1)S(1)}, bf16[2,9,32,128]{3,2,1,0:T(8,128)(2,1)S(1)}, u32[]{:S(2)}, u32[]{:S(2)}) collective-permute-start(bf16[2,9,32,128]{3,2,1,0:T(8,128)(2,1)S(1)} %get-tuple-element.152), channel_id=1, source_target_pairs={{0,14},{1,15},{2,12},{3,13},{4,10},{5,11},{6,8},{7,9},{8,6},{9,7},... | collective-permute-start | bytes 442376 | tf_op jit(solution)/shard_map/ppermute | solution.py:269
  45.8 1.6 %collective-permute-done.14.refs_0_ = bf16[2,9,32,128]{3,2,1,0:T(8,128)(2,1)S(1)} collective-permute-done((bf16[2,9,32,128]{3,2,1,0:T(8,128)(2,1)S(1)}, bf16[2,9,32,128]{3,2,1,0:T(8,128)(2,1)S(1)}, u32[]{:S(2)}, u32[]{:S(2)}) %collective-permute-start.14) | collective-permute-done | bytes 147488 | tf_op jit(solution)/shard_map/ppermute | solution.py:269
  47.8 1.9 %collective-permute-done.16.refs_2_ = bf16[2,9,32,128]{3,2,1,0:T(8,128)(2,1)S(1)} collective-permute-done((bf16[2,9,32,128]{3,2,1,0:T(8,128)(2,1)S(1)}, bf16[2,9,32,128]{3,2,1,0:T(8,128)(2,1)S(1)}, u32[]{:S(2)}, u32[]{:S(2)}) %collective-permute-start.16) | collective-permute-done | bytes 147488 | tf_op jit(solution)/shard_map/ppermute | solution.py:269
  49.9 2.5 %collective-permute-start.18 = (bf16[2,9,32,128]{3,2,1,0:T(8,128)(2,1)S(1)}, bf16[2,9,32,128]{3,2,1,0:T(8,128)(2,1)S(1)}, u32[]{:S(2)}, u32[]{:S(2)}) collective-permute-start(bf16[2,9,32,128]{3,2,1,0:T(8,128)(2,1)S(1)} %get-tuple-element.149), channel_id=1, source_target_pairs={{0,2},{1,5},{2,0},{3,7},{4,6},{5,1},{6,4},{7,3},{8,10},{9,13},{10,... | collective-permute-start | bytes 442376 | tf_op jit(solution)/shard_map/ppermute | solution.py:269
  52.4 2.0 %collective-permute-start.20 = (bf16[2,9,32,128]{3,2,1,0:T(8,128)(2,1)S(1)}, bf16[2,9,32,128]{3,2,1,0:T(8,128)(2,1)S(1)}, u32[]{:S(2)}, u32[]{:S(2)}) collective-permute-start(bf16[2,9,32,128]{3,2,1,0:T(8,128)(2,1)S(1)} %get-tuple-element.151), channel_id=1, source_target_pairs={{0,8},{1,3},{2,10},{3,1},{4,12},{5,7},{6,14},{7,5},{8,0},{9,11},{1... | collective-permute-start | bytes 442376 | tf_op jit(solution)/shard_map/ppermute | solution.py:269
  54.4 1.3 %collective-permute-start.22 = (bf16[1,32,256]{2,1,0:T(8,128)(2,1)S(1)}, bf16[1,32,256]{2,1,0:T(8,128)(2,1)S(1)}, u32[]{:S(2)}, u32[]{:S(2)}) collective-permute-start(bf16[1,32,256]{2,1,0:T(8,128)(2,1)S(1)} %copy-done.11), channel_id=1, source_target_pairs={{1,3},{3,5},{5,7},{7,9},{9,11},{11,13},{13,15},{15,17},{17,19},{19... | collective-permute-start | bytes 49160 | tf_op jit(solution)/shard_map/ppermute | solution.py:434
  55.7 4.3 %collective-permute-done.22 = bf16[1,32,256]{2,1,0:T(8,128)(2,1)S(1)} collective-permute-done((bf16[1,32,256]{2,1,0:T(8,128)(2,1)S(1)}, bf16[1,32,256]{2,1,0:T(8,128)(2,1)S(1)}, u32[]{:S(2)}, u32[]{:S(2)}) %collective-permute-start.22) | collective-permute-done | bytes 16416 | tf_op jit(solution)/shard_map/ppermute | solution.py:434
  60.2 1.2 collective-permute-start.23
  61.9 0.7 collective-permute-done.24.inner_ref
  62.9 3.4 %collective-permute-done.23.rest_0_ = bf16[9,32,128]{2,1,0:T(8,128)(2,1)S(1)} collective-permute-done((bf16[9,32,128]{2,1,0:T(8,128)(2,1)S(1)}, bf16[9,32,128]{2,1,0:T(8,128)(2,1)S(1)}, u32[]{:S(2)}, u32[]{:S(2)}) %collective-permute-start.23) | collective-permute-done | bytes 73760 | tf_op jit(solution)/shard_map/ppermute | solution.py:265
  66.3 1.6 %shard_map.106 = (bf16[8,32,256]{2,1,0:T(8,128)(2,1)}, bf16[9,32,128]{2,1,0:T(8,128)(2,1)S(1)}, bf16[1,32,256]{2,1,0:T(8,128)(2,1)S(1)}, bf16[1,32,256]{2,1,0:T(8,128)(2,1)S(1)}, bf16[8,32,256]{2,1,0:T(8,128)(2,1)S(1)}) custom-call(s32[12]{0:T(128)S(1)} %copy-done.7, f32[8,32,256]{2,1,0:T(8,128)S(1)} %shard_map.98.near_ref, ...), custom_call_target="tpu_custom_call" | custom-call | tf_op jit(solution)/shard_map/pallas_call | solution.py:440
  68.3 1.3 %collective-permute-start.27 = (bf16[1,32,256]{2,1,0:T(8,128)(2,1)S(1)}, bf16[1,32,256]{2,1,0:T(8,128)(2,1)S(1)}, u32[]{:S(2)}, u32[]{:S(2)}) collective-permute-start(bf16[1,32,256]{2,1,0:T(8,128)(2,1)S(1)} %get-tuple-element.168), channel_id=1, source_target_pairs={{1,3},{3,5},{5,7},{7,9},{9,11},{11,13},{13,15},{15,17},{17,19},{19... | collective-permute-start | bytes 49160 | tf_op jit(solution)/shard_map/ppermute | solution.py:402
  69.6 4.6 %collective-permute-done.27 = bf16[1,32,256]{2,1,0:T(8,128)(2,1)S(1)} collective-permute-done((bf16[1,32,256]{2,1,0:T(8,128)(2,1)S(1)}, bf16[1,32,256]{2,1,0:T(8,128)(2,1)S(1)}, u32[]{:S(2)}, u32[]{:S(2)}) %collective-permute-start.27) | collective-permute-done | bytes 16416 | tf_op jit(solution)/shard_map/ppermute | solution.py:402
  74.2 2.4 %collective-permute-start.30 = (bf16[2,9,32,128]{3,2,1,0:T(8,128)(2,1)S(1)}, bf16[2,9,32,128]{3,2,1,0:T(8,128)(2,1)S(1)}, u32[]{:S(2)}, u32[]{:S(2)}) collective-permute-start(bf16[2,9,32,128]{3,2,1,0:T(8,128)(2,1)S(1)} %shard_map.107.refs_0_), channel_id=1, source_target_pairs={{0,8},{1,3},{2,10},{3,1},{4,12},{5,7},{6,14},{7,5},{8,0},{9,11},{1... | collective-permute-start | bytes 442376 | tf_op jit(solution)/shard_map/ppermute | solution.py:269
  76.7 3.5 %collective-permute-start.28 = (bf16[2,9,32,128]{3,2,1,0:T(8,128)(2,1)S(1)}, bf16[2,9,32,128]{3,2,1,0:T(8,128)(2,1)S(1)}, u32[]{:S(2)}, u32[]{:S(2)}) collective-permute-start(bf16[2,9,32,128]{3,2,1,0:T(8,128)(2,1)S(1)} %shard_map.107.refs_0_), channel_id=1, source_target_pairs={{0,2},{1,5},{2,0},{3,7},{4,6},{5,1},{6,4},{7,3},{8,10},{9,13},{10,... | collective-permute-start | bytes 442376 | tf_op jit(solution)/shard_map/ppermute | solution.py:269
  80.2 0.6 shard_map.108.near_ref
  80.8 0.8 collective-permute-start.34
  81.6 1.4 %collective-permute-done.29.refs_2_ = bf16[2,9,32,128]{3,2,1,0:T(8,128)(2,1)S(1)} collective-permute-done((bf16[2,9,32,128]{3,2,1,0:T(8,128)(2,1)S(1)}, bf16[2,9,32,128]{3,2,1,0:T(8,128)(2,1)S(1)}, u32[]{:S(2)}, u32[]{:S(2)}) %collective-permute-start.29) | collective-permute-done | bytes 147488 | tf_op jit(solution)/shard_map/ppermute | solution.py:269
  83.0 1.1 collective-permute-done.28.refs_1_
  84.2 0.7 collective-permute-start.31
  84.9 1.5 %collective-permute-start.33 = (bf16[2,9,32,128]{3,2,1,0:T(8,128)(2,1)S(1)}, bf16[2,9,32,128]{3,2,1,0:T(8,128)(2,1)S(1)}, u32[]{:S(2)}, u32[]{:S(2)}) collective-permute-start(bf16[2,9,32,128]{3,2,1,0:T(8,128)(2,1)S(1)} %collective-permute-done.29.refs_2_), channel_id=1, source_target_pairs={{0,8},{1,3},{2,10},{3,1},{4,12},{5,7},{6,14},{7,5},{8,0},{9,11},{1... | collective-permute-start | bytes 442376 | tf_op jit(solution)/shard_map/ppermute | solution.py:269
  86.4 2.4 %collective-permute-start.32 = (bf16[2,9,32,128]{3,2,1,0:T(8,128)(2,1)S(1)}, bf16[2,9,32,128]{3,2,1,0:T(8,128)(2,1)S(1)}, u32[]{:S(2)}, u32[]{:S(2)}) collective-permute-start(bf16[2,9,32,128]{3,2,1,0:T(8,128)(2,1)S(1)} %collective-permute-done.30.refs_4_), channel_id=1, source_target_pairs={{0,2},{1,5},{2,0},{3,7},{4,6},{5,1},{6,4},{7,3},{8,10},{9,13},{10,... | collective-permute-start | bytes 442376 | tf_op jit(solution)/shard_map/ppermute | solution.py:269
  88.9 0.5 collective-permute-start.36
  89.4 0.6 collective-permute-done.33.refs_6_
  90.0 2.0 %collective-permute-done.32.refs_5_ = bf16[2,9,32,128]{3,2,1,0:T(8,128)(2,1)S(1)} collective-permute-done((bf16[2,9,32,128]{3,2,1,0:T(8,128)(2,1)S(1)}, bf16[2,9,32,128]{3,2,1,0:T(8,128)(2,1)S(1)}, u32[]{:S(2)}, u32[]{:S(2)}) %collective-permute-start.32) | collective-permute-done | bytes 147488 | tf_op jit(solution)/shard_map/ppermute | solution.py:269
  94.1 3.5 %shard_map.109 = (bf16[4,2,9,32,128]{4,3,2,1,0:T(8,128)(2,1)S(1)}, bf16[4,2,9,32,128]{4,3,2,1,0:T(8,128)(2,1)S(1)}, bf16[4,2,9,32,128]{4,3,2,1,0:T(8,128)(2,1)S(1)}, bf16[4,2,9,32,128]{4,3,2,1,0:T(8,128)(2,1)S(1)}) custom-call(s32[128]{0:T(128)S(1)} %bitcast.5, s32[128]{0:T(128)S(1)} %bitcast.7, bf16[128,96,96]{2,1,0:T(8,128)(2,1)S(1)} %copy-done.1, ...), custom_call_target="tpu_custom_call" | custom-call | flops 75497472 | bytes 10485760 | tf_op jit(solution)/shard_map/pallas_call | solution.py:312
  97.9 1.7 %collective-permute-done.43.swap_ref = bf16[4,2,9,32,128]{4,3,2,1,0:T(8,128)(2,1)S(1)} collective-permute-done((bf16[4,2,9,32,128]{4,3,2,1,0:T(8,128)(2,1)S(1)}, bf16[4,2,9,32,128]{4,3,2,1,0:T(8,128)(2,1)S(1)}, u32[]{:S(2)}, u32[]{:S(2)}) %collective-permute-start.43) | collective-permute-done | bytes 589856 | tf_op jit(solution)/shard_map/ppermute | solution.py:274
  100.1 2.0 %collective-permute-start.44 = (bf16[2,9,32,128]{3,2,1,0:T(8,128)(2,1)S(1)}, bf16[2,9,32,128]{3,2,1,0:T(8,128)(2,1)S(1)}, u32[]{:S(2)}, u32[]{:S(2)}) collective-permute-start(bf16[2,9,32,128]{3,2,1,0:T(8,128)(2,1)S(1)} %get-tuple-element.192), channel_id=1, source_target_pairs={{0,4},{1,9},{2,6},{3,11},{4,0},{5,13},{6,2},{7,15},{8,12},{9,1},{1... | collective-permute-start | bytes 442376 | tf_op jit(solution)/shard_map/ppermute | solution.py:269
  102.2 0.8 collective-permute-start.45
  102.9 2.0 %collective-permute-start.46 = (bf16[2,9,32,128]{3,2,1,0:T(8,128)(2,1)S(1)}, bf16[2,9,32,128]{3,2,1,0:T(8,128)(2,1)S(1)}, u32[]{:S(2)}, u32[]{:S(2)}) collective-permute-start(bf16[2,9,32,128]{3,2,1,0:T(8,128)(2,1)S(1)} %get-tuple-element.194), channel_id=1, source_target_pairs={{0,2},{1,5},{2,0},{3,7},{4,6},{5,1},{6,4},{7,3},{8,10},{9,13},{10,... | collective-permute-start | bytes 442376 | tf_op jit(solution)/shard_map/ppermute | solution.py:269
  104.9 0.7 collective-permute-start.47
  105.6 2.3 %collective-permute-done.45.refs_1_ = bf16[2,9,32,128]{3,2,1,0:T(8,128)(2,1)S(1)} collective-permute-done((bf16[2,9,32,128]{3,2,1,0:T(8,128)(2,1)S(1)}, bf16[2,9,32,128]{3,2,1,0:T(8,128)(2,1)S(1)}, u32[]{:S(2)}, u32[]{:S(2)}) %collective-permute-start.45) | collective-permute-done | bytes 147488 | tf_op jit(solution)/shard_map/ppermute | solution.py:269
  108.0 1.0 collective-permute-done.46.refs_2_
  109.0 2.0 %collective-permute-done.47.refs_3_ = bf16[2,9,32,128]{3,2,1,0:T(8,128)(2,1)S(1)} collective-permute-done((bf16[2,9,32,128]{3,2,1,0:T(8,128)(2,1)S(1)}, bf16[2,9,32,128]{3,2,1,0:T(8,128)(2,1)S(1)}, u32[]{:S(2)}, u32[]{:S(2)}) %collective-permute-start.47) | collective-permute-done | bytes 147488 | tf_op jit(solution)/shard_map/ppermute | solution.py:269
  111.2 1.8 %collective-permute-start.49 = (bf16[2,9,32,128]{3,2,1,0:T(8,128)(2,1)S(1)}, bf16[2,9,32,128]{3,2,1,0:T(8,128)(2,1)S(1)}, u32[]{:S(2)}, u32[]{:S(2)}) collective-permute-start(bf16[2,9,32,128]{3,2,1,0:T(8,128)(2,1)S(1)} %get-tuple-element.209), channel_id=1, source_target_pairs={{0,2},{1,5},{2,0},{3,7},{4,6},{5,1},{6,4},{7,3},{8,10},{9,13},{10,... | collective-permute-start | bytes 442376 | tf_op jit(solution)/shard_map/ppermute | solution.py:269
  113.0 1.2 collective-permute-start.50
  114.2 0.8 collective-permute-start.51
  115.0 2.7 %collective-permute-done.49.refs_0_ = bf16[2,9,32,128]{3,2,1,0:T(8,128)(2,1)S(1)} collective-permute-done((bf16[2,9,32,128]{3,2,1,0:T(8,128)(2,1)S(1)}, bf16[2,9,32,128]{3,2,1,0:T(8,128)(2,1)S(1)}, u32[]{:S(2)}, u32[]{:S(2)}) %collective-permute-start.49) | collective-permute-done | bytes 147488 | tf_op jit(solution)/shard_map/ppermute | solution.py:269
  118.2 1.2 collective-permute-done.51.refs_2_
  119.4 1.7 %collective-permute-start.52 = (bf16[9,32,128]{2,1,0:T(8,128)(2,1)S(1)}, bf16[9,32,128]{2,1,0:T(8,128)(2,1)S(1)}, u32[]{:S(2)}, u32[]{:S(2)}) collective-permute-start(bf16[9,32,128]{2,1,0:T(8,128)(2,1)S(1)} %get-tuple-element.218), channel_id=1, source_target_pairs={{0,16},{1,17},{2,18},{3,19},{4,20},{5,21},{6,22},{7,23},{8,24},{9,... | collective-permute-start | bytes 221192 | tf_op jit(solution)/shard_map/ppermute | solution.py:265
  121.6 0.7 collective-permute-done.53.inner_ref
  122.6 2.9 %collective-permute-done.52.rest_0_ = bf16[9,32,128]{2,1,0:T(8,128)(2,1)S(1)} collective-permute-done((bf16[9,32,128]{2,1,0:T(8,128)(2,1)S(1)}, bf16[9,32,128]{2,1,0:T(8,128)(2,1)S(1)}, u32[]{:S(2)}, u32[]{:S(2)}) %collective-permute-start.52) | collective-permute-done | bytes 73760 | tf_op jit(solution)/shard_map/ppermute | solution.py:265
  125.5 1.6 %shard_map.114 = bf16[8,32,256]{2,1,0:T(8,128)(2,1)} custom-call(s32[12]{0:T(128)S(1)} %copy-done.7, f32[8,32,256]{2,1,0:T(8,128)S(1)} %shard_map.108.near_ref, f32[2,32,256]{2,1,0:T(8,128)S(1)} %shard_map.113.edge_ref, bf16[8,96,256]{2,1,0:T(8,128)(2,1)S(1)} %copy-done.2, bf16[8,96,96]{2,1,0:T(8,128)(2,1)S(1)} %copy-done.3, ...), custom_call_target="tpu_custom_call" | custom-call | tf_op jit(solution)/shard_map/pallas_call | solution.py:440
  (91 shorter events, 11.5 us)
Async XLA Ops:
  3.5 9.5 %copy-start.5 = (bf16[9,32,128]{2,1,0:T(8,128)(2,1)S(1)}, bf16[9,32,128]{2,1,0:T(8,128)(2,1)}, u32[]{:S(2)}) copy-start(bf16[9,32,128]{2,1,0:T(8,128)(2,1)} %get-tuple-element.113.__.refs_0_) | copy-start | bytes 221188
  3.5 15.0 %copy-start = (bf16[8,3,256,256]{3,2,1,0:T(8,128)(2,1)S(1)}, bf16[8,3,256,256]{3,2,1,0:T(8,128)(2,1)}, u32[]{:S(2)}) copy-start(bf16[8,3,256,256]{3,2,1,0:T(8,128)(2,1)} %last_ref.3) | copy-start | bytes 9437188
  3.6 15.0 %copy-start.4 = (bf16[8,32,256]{2,1,0:T(8,128)(2,1)S(1)}, bf16[8,32,256]{2,1,0:T(8,128)(2,1)}, u32[]{:S(2)}) copy-start(bf16[8,32,256]{2,1,0:T(8,128)(2,1)} %v_ref.1) | copy-start | bytes 393220
  3.6 9.5 %collective-permute-start = (bf16[9,32,128]{2,1,0:T(8,128)(2,1)}, bf16[9,32,128]{2,1,0:T(8,128)(2,1)S(1)}, u32[]{:S(2)}, u32[]{:S(2)}) collective-permute-start(bf16[9,32,128]{2,1,0:T(8,128)(2,1)} %get-tuple-element.113.__.refs_0_), channel_id=1, source_target_pairs={{0,16},{1,17},{2,18},{3,19},{4,20},{5,21},{6,22},{7,23},{8,24},{9,... | collective-permute-start | bytes 221192 | tf_op jit(solution)/shard_map/ppermute | solution.py:265
  13.0 21.9 %copy-start.1 = (bf16[128,96,96]{2,1,0:T(8,128)(2,1)S(1)}, bf16[128,96,96]{2,1,0:T(8,128)(2,1)}, u32[]{:S(2)}) copy-start(bf16[128,96,96]{2,1,0:T(8,128)(2,1)} %copy.10._.coupling_ref) | copy-start | bytes 7077892
  13.9 19.7 %copy-start.8 = (s32[128]{0:T(128)S(1)}, s32[128]{0:T(128)}, u32[]{:S(2)}) copy-start(s32[128]{0:T(128)} %param.14) | copy-start | bytes 1540
  13.9 19.7 %copy-start.9 = (s32[128]{0:T(128)S(1)}, s32[128]{0:T(128)}, u32[]{:S(2)}) copy-start(s32[128]{0:T(128)} %param.15) | copy-start | bytes 1540
  13.9 6.6 %collective-permute-start.3 = (bf16[2,9,32,128]{3,2,1,0:T(8,128)(2,1)S(1)}, bf16[2,9,32,128]{3,2,1,0:T(8,128)(2,1)S(1)}, u32[]{:S(2)}, u32[]{:S(2)}) collective-permute-start(bf16[2,9,32,128]{3,2,1,0:T(8,128)(2,1)S(1)} %shard_map.97.refs_0_), channel_id=1, source_target_pairs={{0,8},{1,3},{2,10},{3,1},{4,12},{5,7},{6,14},{7,5},{8,0},{9,11},{1... | collective-permute-start | bytes 442376 | tf_op jit(solution)/shard_map/ppermute | solution.py:269
  15.5 6.2 %collective-permute-start.2 = (bf16[2,9,32,128]{3,2,1,0:T(8,128)(2,1)S(1)}, bf16[2,9,32,128]{3,2,1,0:T(8,128)(2,1)S(1)}, u32[]{:S(2)}, u32[]{:S(2)}) collective-permute-start(bf16[2,9,32,128]{3,2,1,0:T(8,128)(2,1)S(1)} %shard_map.97.refs_0_), channel_id=1, source_target_pairs={{0,4},{1,9},{2,6},{3,11},{4,0},{5,13},{6,2},{7,15},{8,12},{9,1},{1... | collective-permute-start | bytes 442376 | tf_op jit(solution)/shard_map/ppermute | solution.py:269
  17.0 5.1 %collective-permute-start.1 = (bf16[2,9,32,128]{3,2,1,0:T(8,128)(2,1)S(1)}, bf16[2,9,32,128]{3,2,1,0:T(8,128)(2,1)S(1)}, u32[]{:S(2)}, u32[]{:S(2)}) collective-permute-start(bf16[2,9,32,128]{3,2,1,0:T(8,128)(2,1)S(1)} %shard_map.97.refs_0_), channel_id=1, source_target_pairs={{0,2},{1,5},{2,0},{3,7},{4,6},{5,1},{6,4},{7,3},{8,10},{9,13},{10,... | collective-permute-start | bytes 442376 | tf_op jit(solution)/shard_map/ppermute | solution.py:269
  22.2 10.3 %collective-permute-start.8 = (bf16[4,2,9,32,128]{4,3,2,1,0:T(8,128)(2,1)S(1)}, bf16[4,2,9,32,128]{4,3,2,1,0:T(8,128)(2,1)S(1)}, u32[]{:S(2)}, u32[]{:S(2)}) collective-permute-start(bf16[4,2,9,32,128]{4,3,2,1,0:T(8,128)(2,1)S(1)} %shard_map.100.refs_0_), channel_id=1, source_target_pairs={{0,1},{1,0},{2,3},{3,2},{4,5},{5,4},{6,7},{7,6},{8,9},{9,8},{10,11... | collective-permute-start | bytes 1769480 | tf_op jit(solution)/shard_map/ppermute | solution.py:274
  22.3 5.9 %collective-permute-start.6 = (bf16[2,9,32,128]{3,2,1,0:T(8,128)(2,1)S(1)}, bf16[2,9,32,128]{3,2,1,0:T(8,128)(2,1)S(1)}, u32[]{:S(2)}, u32[]{:S(2)}) collective-permute-start(bf16[2,9,32,128]{3,2,1,0:T(8,128)(2,1)S(1)} %collective-permute-done.2.refs_2_), channel_id=1, source_target_pairs={{0,8},{1,3},{2,10},{3,1},{4,12},{5,7},{6,14},{7,5},{8,0},{9,11},{1... | collective-permute-start | bytes 442376 | tf_op jit(solution)/shard_map/ppermute | solution.py:269
  22.8 5.7 %collective-permute-start.7 = (bf16[2,9,32,128]{3,2,1,0:T(8,128)(2,1)S(1)}, bf16[2,9,32,128]{3,2,1,0:T(8,128)(2,1)S(1)}, u32[]{:S(2)}, u32[]{:S(2)}) collective-permute-start(bf16[2,9,32,128]{3,2,1,0:T(8,128)(2,1)S(1)} %collective-permute-done.3.refs_3_), channel_id=1, source_target_pairs={{0,2},{1,5},{2,0},{3,7},{4,6},{5,1},{6,4},{7,3},{8,10},{9,13},{10,... | collective-permute-start | bytes 442376 | tf_op jit(solution)/shard_map/ppermute | solution.py:269
  24.3 5.9 %collective-permute-start.5 = (bf16[2,9,32,128]{3,2,1,0:T(8,128)(2,1)S(1)}, bf16[2,9,32,128]{3,2,1,0:T(8,128)(2,1)S(1)}, u32[]{:S(2)}, u32[]{:S(2)}) collective-permute-start(bf16[2,9,32,128]{3,2,1,0:T(8,128)(2,1)S(1)} %collective-permute-done.1.refs_1_), channel_id=1, source_target_pairs={{0,4},{1,9},{2,6},{3,11},{4,0},{5,13},{6,2},{7,15},{8,12},{9,1},{1... | collective-permute-start | bytes 442376 | tf_op jit(solution)/shard_map/ppermute | solution.py:269
  24.8 7.7 %collective-permute-start.4 = (bf16[2,9,32,128]{3,2,1,0:T(8,128)(2,1)S(1)}, bf16[2,9,32,128]{3,2,1,0:T(8,128)(2,1)S(1)}, u32[]{:S(2)}, u32[]{:S(2)}) collective-permute-start(bf16[2,9,32,128]{3,2,1,0:T(8,128)(2,1)S(1)} %collective-permute-done.1.refs_1_), channel_id=1, source_target_pairs={{0,12},{1,11},{2,14},{3,9},{4,8},{5,15},{6,10},{7,13},{8,4},{9,3},... | collective-permute-start | bytes 442376 | tf_op jit(solution)/shard_map/ppermute | solution.py:269
  32.5 1.5 %collective-permute-start.9 = (bf16[2,9,32,128]{3,2,1,0:T(8,128)(2,1)S(1)}, bf16[2,9,32,128]{3,2,1,0:T(8,128)(2,1)S(1)}, u32[]{:S(2)}, u32[]{:S(2)}) collective-permute-start(bf16[2,9,32,128]{3,2,1,0:T(8,128)(2,1)S(1)} %collective-permute-done.4.refs_1_), channel_id=1, source_target_pairs={{0,1},{1,0},{2,3},{3,2},{4,5},{5,4},{6,7},{7,6},{8,9},{9,8},{10,11... | collective-permute-start | bytes 442376 | tf_op jit(solution)/shard_map/ppermute | solution.py:274
  33.0 1.4 %collective-permute-start.10 = (bf16[2,9,32,128]{3,2,1,0:T(8,128)(2,1)S(1)}, bf16[2,9,32,128]{3,2,1,0:T(8,128)(2,1)S(1)}, u32[]{:S(2)}, u32[]{:S(2)}) collective-permute-start(bf16[2,9,32,128]{3,2,1,0:T(8,128)(2,1)S(1)} %collective-permute-done.5.refs_2_), channel_id=1, source_target_pairs={{0,1},{1,0},{2,3},{3,2},{4,5},{5,4},{6,7},{7,6},{8,9},{9,8},{10,11... | collective-permute-start | bytes 442376 | tf_op jit(solution)/shard_map/ppermute | solution.py:274
  33.0 1.6 %collective-permute-start.11 = (bf16[2,9,32,128]{3,2,1,0:T(8,128)(2,1)S(1)}, bf16[2,9,32,128]{3,2,1,0:T(8,128)(2,1)S(1)}, u32[]{:S(2)}, u32[]{:S(2)}) collective-permute-start(bf16[2,9,32,128]{3,2,1,0:T(8,128)(2,1)S(1)} %collective-permute-done.6.refs_3_), channel_id=1, source_target_pairs={{0,1},{1,0},{2,3},{3,2},{4,5},{5,4},{6,7},{7,6},{8,9},{9,8},{10,11... | collective-permute-start | bytes 442376 | tf_op jit(solution)/shard_map/ppermute | solution.py:274
  33.5 1.4 %collective-permute-start.12 = (bf16[2,9,32,128]{3,2,1,0:T(8,128)(2,1)S(1)}, bf16[2,9,32,128]{3,2,1,0:T(8,128)(2,1)S(1)}, u32[]{:S(2)}, u32[]{:S(2)}) collective-permute-start(bf16[2,9,32,128]{3,2,1,0:T(8,128)(2,1)S(1)} %collective-permute-done.7.refs_4_), channel_id=1, source_target_pairs={{0,1},{1,0},{2,3},{3,2},{4,5},{5,4},{6,7},{7,6},{8,9},{9,8},{10,11... | collective-permute-start | bytes 442376 | tf_op jit(solution)/shard_map/ppermute | solution.py:274
  34.9 19.5 %copy-start.11 = (bf16[1,32,256]{2,1,0:T(8,128)(2,1)S(1)}, bf16[1,32,256]{2,1,0:T(8,128)(2,1)}, u32[]{:S(2)}) copy-start(bf16[1,32,256]{2,1,0:T(8,128)(2,1)} %get-tuple-element.154) | copy-start | bytes 49156
  38.4 23.0 %copy-start.10 = (bf16[1,32,256]{2,1,0:T(8,128)(2,1)S(1)}, bf16[1,32,256]{2,1,0:T(8,128)(2,1)}, u32[]{:S(2)}) copy-start(bf16[1,32,256]{2,1,0:T(8,128)(2,1)} %get-tuple-element.161) | copy-start | bytes 49156
  38.4 2.1 %collective-permute-start.13 = (bf16[4,2,9,32,128]{4,3,2,1,0:T(8,128)(2,1)S(1)}, bf16[4,2,9,32,128]{4,3,2,1,0:T(8,128)(2,1)S(1)}, u32[]{:S(2)}, u32[]{:S(2)}) collective-permute-start(bf16[4,2,9,32,128]{4,3,2,1,0:T(8,128)(2,1)S(1)} %get-tuple-element.128), channel_id=1, source_target_pairs={{0,1},{1,0},{2,3},{3,2},{4,5},{5,4},{6,7},{7,6},{8,9},{9,8},{10,11... | collective-permute-start | bytes 1769480 | tf_op jit(solution)/shard_map/ppermute | solution.py:274
  40.6 9.1 %collective-permute-start.17 = (bf16[4,2,9,32,128]{4,3,2,1,0:T(8,128)(2,1)S(1)}, bf16[4,2,9,32,128]{4,3,2,1,0:T(8,128)(2,1)S(1)}, u32[]{:S(2)}, u32[]{:S(2)}) collective-permute-start(bf16[4,2,9,32,128]{4,3,2,1,0:T(8,128)(2,1)S(1)} %get-tuple-element.137), channel_id=1, source_target_pairs={{0,1},{1,0},{2,3},{3,2},{4,5},{5,4},{6,7},{7,6},{8,9},{9,8},{10,11... | collective-permute-start | bytes 1769480 | tf_op jit(solution)/shard_map/ppermute | solution.py:274
  40.9 6.6 %collective-permute-start.14 = (bf16[2,9,32,128]{3,2,1,0:T(8,128)(2,1)S(1)}, bf16[2,9,32,128]{3,2,1,0:T(8,128)(2,1)S(1)}, u32[]{:S(2)}, u32[]{:S(2)}) collective-permute-start(bf16[2,9,32,128]{3,2,1,0:T(8,128)(2,1)S(1)} %get-tuple-element.134), channel_id=1, source_target_pairs={{0,4},{1,9},{2,6},{3,11},{4,0},{5,13},{6,2},{7,15},{8,12},{9,1},{1... | collective-permute-start | bytes 442376 | tf_op jit(solution)/shard_map/ppermute | solution.py:269
  41.9 5.9 %collective-permute-start.15 = (bf16[2,9,32,128]{3,2,1,0:T(8,128)(2,1)S(1)}, bf16[2,9,32,128]{3,2,1,0:T(8,128)(2,1)S(1)}, u32[]{:S(2)}, u32[]{:S(2)}) collective-permute-start(bf16[2,9,32,128]{3,2,1,0:T(8,128)(2,1)S(1)} %get-tuple-element.135), channel_id=1, source_target_pairs={{0,8},{1,3},{2,10},{3,1},{4,12},{5,7},{6,14},{7,5},{8,0},{9,11},{1... | collective-permute-start | bytes 442376 | tf_op jit(solution)/shard_map/ppermute | solution.py:269
  42.3 7.3 %collective-permute-start.16 = (bf16[2,9,32,128]{3,2,1,0:T(8,128)(2,1)S(1)}, bf16[2,9,32,128]{3,2,1,0:T(8,128)(2,1)S(1)}, u32[]{:S(2)}, u32[]{:S(2)}) collective-permute-start(bf16[2,9,32,128]{3,2,1,0:T(8,128)(2,1)S(1)} %get-tuple-element.136), channel_id=1, source_target_pairs={{0,2},{1,5},{2,0},{3,7},{4,6},{5,1},{6,4},{7,3},{8,10},{9,13},{10,... | collective-permute-start | bytes 442376 | tf_op jit(solution)/shard_map/ppermute | solution.py:269
  43.8 11.9 %collective-permute-start.21 = (bf16[2,9,32,128]{3,2,1,0:T(8,128)(2,1)S(1)}, bf16[2,9,32,128]{3,2,1,0:T(8,128)(2,1)S(1)}, u32[]{:S(2)}, u32[]{:S(2)}) collective-permute-start(bf16[2,9,32,128]{3,2,1,0:T(8,128)(2,1)S(1)} %get-tuple-element.152), channel_id=1, source_target_pairs={{0,14},{1,15},{2,12},{3,13},{4,10},{5,11},{6,8},{7,9},{8,6},{9,7},... | collective-permute-start | bytes 442376 | tf_op jit(solution)/shard_map/ppermute | solution.py:269
  49.9 10.2 %collective-permute-start.18 = (bf16[2,9,32,128]{3,2,1,0:T(8,128)(2,1)S(1)}, bf16[2,9,32,128]{3,2,1,0:T(8,128)(2,1)S(1)}, u32[]{:S(2)}, u32[]{:S(2)}) collective-permute-start(bf16[2,9,32,128]{3,2,1,0:T(8,128)(2,1)S(1)} %get-tuple-element.149), channel_id=1, source_target_pairs={{0,2},{1,5},{2,0},{3,7},{4,6},{5,1},{6,4},{7,3},{8,10},{9,13},{10,... | collective-permute-start | bytes 442376 | tf_op jit(solution)/shard_map/ppermute | solution.py:269
  52.4 7.7 %collective-permute-start.19 = (bf16[2,9,32,128]{3,2,1,0:T(8,128)(2,1)S(1)}, bf16[2,9,32,128]{3,2,1,0:T(8,128)(2,1)S(1)}, u32[]{:S(2)}, u32[]{:S(2)}) collective-permute-start(bf16[2,9,32,128]{3,2,1,0:T(8,128)(2,1)S(1)} %get-tuple-element.150), channel_id=1, source_target_pairs={{0,4},{1,9},{2,6},{3,11},{4,0},{5,13},{6,2},{7,15},{8,12},{9,1},{1... | collective-permute-start | bytes 442376 | tf_op jit(solution)/shard_map/ppermute | solution.py:269
  52.4 7.7 %collective-permute-start.20 = (bf16[2,9,32,128]{3,2,1,0:T(8,128)(2,1)S(1)}, bf16[2,9,32,128]{3,2,1,0:T(8,128)(2,1)S(1)}, u32[]{:S(2)}, u32[]{:S(2)}) collective-permute-start(bf16[2,9,32,128]{3,2,1,0:T(8,128)(2,1)S(1)} %get-tuple-element.151), channel_id=1, source_target_pairs={{0,8},{1,3},{2,10},{3,1},{4,12},{5,7},{6,14},{7,5},{8,0},{9,11},{1... | collective-permute-start | bytes 442376 | tf_op jit(solution)/shard_map/ppermute | solution.py:269
  54.4 5.6 %collective-permute-start.22 = (bf16[1,32,256]{2,1,0:T(8,128)(2,1)S(1)}, bf16[1,32,256]{2,1,0:T(8,128)(2,1)S(1)}, u32[]{:S(2)}, u32[]{:S(2)}) collective-permute-start(bf16[1,32,256]{2,1,0:T(8,128)(2,1)S(1)} %copy-done.11), channel_id=1, source_target_pairs={{1,3},{3,5},{5,7},{7,9},{9,11},{11,13},{13,15},{15,17},{17,19},{19... | collective-permute-start | bytes 49160 | tf_op jit(solution)/shard_map/ppermute | solution.py:434
  60.1 6.1 %copy-start.2 = (bf16[8,96,256]{2,1,0:T(8,128)(2,1)S(1)}, bf16[8,96,256]{2,1,0:T(8,128)(2,1)}, u32[]{:S(2)}) copy-start(bf16[8,96,256]{2,1,0:T(8,128)(2,1)} %basis_ref.3) | copy-start | bytes 1179652
  60.2 6.1 %collective-permute-start.23 = (bf16[9,32,128]{2,1,0:T(8,128)(2,1)S(1)}, bf16[9,32,128]{2,1,0:T(8,128)(2,1)S(1)}, u32[]{:S(2)}, u32[]{:S(2)}) collective-permute-start(bf16[9,32,128]{2,1,0:T(8,128)(2,1)S(1)} %get-tuple-element.160), channel_id=1, source_target_pairs={{0,16},{1,17},{2,18},{3,19},{4,20},{5,21},{6,22},{7,23},{8,24},{9,... | collective-permute-start | bytes 221192 | tf_op jit(solution)/shard_map/ppermute | solution.py:265
  61.4 1.2 collective-permute-start.24
  61.4 1.3 %collective-permute-start.25 = (bf16[1,32,256]{2,1,0:T(8,128)(2,1)S(1)}, bf16[1,32,256]{2,1,0:T(8,128)(2,1)S(1)}, u32[]{:S(2)}, u32[]{:S(2)}) collective-permute-start(bf16[1,32,256]{2,1,0:T(8,128)(2,1)S(1)} %collective-permute-done.22), channel_id=1, source_target_pairs={{0,1},{1,0},{2,3},{3,2},{4,5},{5,4},{6,7},{7,6},{8,9},{9,8},{10,11... | collective-permute-start | bytes 49160 | tf_op jit(solution)/shard_map/ppermute | solution.py:274
  67.9 6.3 %collective-permute-start.26 = (bf16[9,32,128]{2,1,0:T(8,128)(2,1)S(1)}, bf16[9,32,128]{2,1,0:T(8,128)(2,1)S(1)}, u32[]{:S(2)}, u32[]{:S(2)}) collective-permute-start(bf16[9,32,128]{2,1,0:T(8,128)(2,1)S(1)} %get-tuple-element.167.refs_0_), channel_id=1, source_target_pairs={{0,16},{1,17},{2,18},{3,19},{4,20},{5,21},{6,22},{7,23},{8,24},{9,... | collective-permute-start | bytes 221192 | tf_op jit(solution)/shard_map/ppermute | solution.py:265
  68.3 5.9 %collective-permute-start.27 = (bf16[1,32,256]{2,1,0:T(8,128)(2,1)S(1)}, bf16[1,32,256]{2,1,0:T(8,128)(2,1)S(1)}, u32[]{:S(2)}, u32[]{:S(2)}) collective-permute-start(bf16[1,32,256]{2,1,0:T(8,128)(2,1)S(1)} %get-tuple-element.168), channel_id=1, source_target_pairs={{1,3},{3,5},{5,7},{7,9},{9,11},{11,13},{13,15},{15,17},{17,19},{19... | collective-permute-start | bytes 49160 | tf_op jit(solution)/shard_map/ppermute | solution.py:402
  74.2 7.4 %collective-permute-start.30 = (bf16[2,9,32,128]{3,2,1,0:T(8,128)(2,1)S(1)}, bf16[2,9,32,128]{3,2,1,0:T(8,128)(2,1)S(1)}, u32[]{:S(2)}, u32[]{:S(2)}) collective-permute-start(bf16[2,9,32,128]{3,2,1,0:T(8,128)(2,1)S(1)} %shard_map.107.refs_0_), channel_id=1, source_target_pairs={{0,8},{1,3},{2,10},{3,1},{4,12},{5,7},{6,14},{7,5},{8,0},{9,11},{1... | collective-permute-start | bytes 442376 | tf_op jit(solution)/shard_map/ppermute | solution.py:269
  76.7 6.3 %collective-permute-start.29 = (bf16[2,9,32,128]{3,2,1,0:T(8,128)(2,1)S(1)}, bf16[2,9,32,128]{3,2,1,0:T(8,128)(2,1)S(1)}, u32[]{:S(2)}, u32[]{:S(2)}) collective-permute-start(bf16[2,9,32,128]{3,2,1,0:T(8,128)(2,1)S(1)} %shard_map.107.refs_0_), channel_id=1, source_target_pairs={{0,4},{1,9},{2,6},{3,11},{4,0},{5,13},{6,2},{7,15},{8,12},{9,1},{1... | collective-permute-start | bytes 442376 | tf_op jit(solution)/shard_map/ppermute | solution.py:269
  76.7 7.5 %collective-permute-start.28 = (bf16[2,9,32,128]{3,2,1,0:T(8,128)(2,1)S(1)}, bf16[2,9,32,128]{3,2,1,0:T(8,128)(2,1)S(1)}, u32[]{:S(2)}, u32[]{:S(2)}) collective-permute-start(bf16[2,9,32,128]{3,2,1,0:T(8,128)(2,1)S(1)} %shard_map.107.refs_0_), channel_id=1, source_target_pairs={{0,2},{1,5},{2,0},{3,7},{4,6},{5,1},{6,4},{7,3},{8,10},{9,13},{10,... | collective-permute-start | bytes 442376 | tf_op jit(solution)/shard_map/ppermute | solution.py:269
  80.8 8.1 %collective-permute-start.34 = (bf16[2,9,32,128]{3,2,1,0:T(8,128)(2,1)S(1)}, bf16[2,9,32,128]{3,2,1,0:T(8,128)(2,1)S(1)}, u32[]{:S(2)}, u32[]{:S(2)}) collective-permute-start(bf16[2,9,32,128]{3,2,1,0:T(8,128)(2,1)S(1)} %shard_map.107.refs_0_), channel_id=1, source_target_pairs={{0,14},{1,15},{2,12},{3,13},{4,10},{5,11},{6,8},{7,9},{8,6},{9,7},... | collective-permute-start | bytes 442376 | tf_op jit(solution)/shard_map/ppermute | solution.py:269
  84.2 5.2 %collective-permute-start.31 = (bf16[2,9,32,128]{3,2,1,0:T(8,128)(2,1)S(1)}, bf16[2,9,32,128]{3,2,1,0:T(8,128)(2,1)S(1)}, u32[]{:S(2)}, u32[]{:S(2)}) collective-permute-start(bf16[2,9,32,128]{3,2,1,0:T(8,128)(2,1)S(1)} %collective-permute-done.28.refs_1_), channel_id=1, source_target_pairs={{0,4},{1,9},{2,6},{3,11},{4,0},{5,13},{6,2},{7,15},{8,12},{9,1},{1... | collective-permute-start | bytes 442376 | tf_op jit(solution)/shard_map/ppermute | solution.py:269
  84.9 5.1 %collective-permute-start.33 = (bf16[2,9,32,128]{3,2,1,0:T(8,128)(2,1)S(1)}, bf16[2,9,32,128]{3,2,1,0:T(8,128)(2,1)S(1)}, u32[]{:S(2)}, u32[]{:S(2)}) collective-permute-start(bf16[2,9,32,128]{3,2,1,0:T(8,128)(2,1)S(1)} %collective-permute-done.29.refs_2_), channel_id=1, source_target_pairs={{0,8},{1,3},{2,10},{3,1},{4,12},{5,7},{6,14},{7,5},{8,0},{9,11},{1... | collective-permute-start | bytes 442376 | tf_op jit(solution)/shard_map/ppermute | solution.py:269
  86.4 5.6 %collective-permute-start.32 = (bf16[2,9,32,128]{3,2,1,0:T(8,128)(2,1)S(1)}, bf16[2,9,32,128]{3,2,1,0:T(8,128)(2,1)S(1)}, u32[]{:S(2)}, u32[]{:S(2)}) collective-permute-start(bf16[2,9,32,128]{3,2,1,0:T(8,128)(2,1)S(1)} %collective-permute-done.30.refs_4_), channel_id=1, source_target_pairs={{0,2},{1,5},{2,0},{3,7},{4,6},{5,1},{6,4},{7,3},{8,10},{9,13},{10,... | collective-permute-start | bytes 442376 | tf_op jit(solution)/shard_map/ppermute | solution.py:269
  88.9 3.1 %collective-permute-start.35 = (bf16[2,9,32,128]{3,2,1,0:T(8,128)(2,1)S(1)}, bf16[2,9,32,128]{3,2,1,0:T(8,128)(2,1)S(1)}, u32[]{:S(2)}, u32[]{:S(2)}) collective-permute-start(bf16[2,9,32,128]{3,2,1,0:T(8,128)(2,1)S(1)} %shard_map.107.refs_0_), channel_id=1, source_target_pairs={{0,1},{1,0},{2,3},{3,2},{4,5},{5,4},{6,7},{7,6},{8,9},{9,8},{10,11... | collective-permute-start | bytes 442376 | tf_op jit(solution)/shard_map/ppermute | solution.py:274
  88.9 3.6 %collective-permute-start.36 = (bf16[2,9,32,128]{3,2,1,0:T(8,128)(2,1)S(1)}, bf16[2,9,32,128]{3,2,1,0:T(8,128)(2,1)S(1)}, u32[]{:S(2)}, u32[]{:S(2)}) collective-permute-start(bf16[2,9,32,128]{3,2,1,0:T(8,128)(2,1)S(1)} %collective-permute-done.28.refs_1_), channel_id=1, source_target_pairs={{0,1},{1,0},{2,3},{3,2},{4,5},{5,4},{6,7},{7,6},{8,9},{9,8},{10,11... | collective-permute-start | bytes 442376 | tf_op jit(solution)/shard_map/ppermute | solution.py:274
  89.4 3.2 %collective-permute-start.37 = (bf16[2,9,32,128]{3,2,1,0:T(8,128)(2,1)S(1)}, bf16[2,9,32,128]{3,2,1,0:T(8,128)(2,1)S(1)}, u32[]{:S(2)}, u32[]{:S(2)}) collective-permute-start(bf16[2,9,32,128]{3,2,1,0:T(8,128)(2,1)S(1)} %collective-permute-done.29.refs_2_), channel_id=1, source_target_pairs={{0,1},{1,0},{2,3},{3,2},{4,5},{5,4},{6,7},{7,6},{8,9},{9,8},{10,11... | collective-permute-start | bytes 442376 | tf_op jit(solution)/shard_map/ppermute | solution.py:274
  90.0 3.0 %collective-permute-start.39 = (bf16[2,9,32,128]{3,2,1,0:T(8,128)(2,1)S(1)}, bf16[2,9,32,128]{3,2,1,0:T(8,128)(2,1)S(1)}, u32[]{:S(2)}, u32[]{:S(2)}) collective-permute-start(bf16[2,9,32,128]{3,2,1,0:T(8,128)(2,1)S(1)} %collective-permute-done.30.refs_4_), channel_id=1, source_target_pairs={{0,1},{1,0},{2,3},{3,2},{4,5},{5,4},{6,7},{7,6},{8,9},{9,8},{10,11... | collective-permute-start | bytes 442376 | tf_op jit(solution)/shard_map/ppermute | solution.py:274
  92.0 1.4 %collective-permute-start.38 = (bf16[2,9,32,128]{3,2,1,0:T(8,128)(2,1)S(1)}, bf16[2,9,32,128]{3,2,1,0:T(8,128)(2,1)S(1)}, u32[]{:S(2)}, u32[]{:S(2)}) collective-permute-start(bf16[2,9,32,128]{3,2,1,0:T(8,128)(2,1)S(1)} %collective-permute-done.31.refs_3_), channel_id=1, source_target_pairs={{0,1},{1,0},{2,3},{3,2},{4,5},{5,4},{6,7},{7,6},{8,9},{9,8},{10,11... | collective-permute-start | bytes 442376 | tf_op jit(solution)/shard_map/ppermute | solution.py:274
  92.0 1.6 %collective-permute-start.40 = (bf16[2,9,32,128]{3,2,1,0:T(8,128)(2,1)S(1)}, bf16[2,9,32,128]{3,2,1,0:T(8,128)(2,1)S(1)}, u32[]{:S(2)}, u32[]{:S(2)}) collective-permute-start(bf16[2,9,32,128]{3,2,1,0:T(8,128)(2,1)S(1)} %collective-permute-done.32.refs_5_), channel_id=1, source_target_pairs={{0,1},{1,0},{2,3},{3,2},{4,5},{5,4},{6,7},{7,6},{8,9},{9,8},{10,11... | collective-permute-start | bytes 442376 | tf_op jit(solution)/shard_map/ppermute | solution.py:274
  92.5 1.4 %collective-permute-start.41 = (bf16[2,9,32,128]{3,2,1,0:T(8,128)(2,1)S(1)}, bf16[2,9,32,128]{3,2,1,0:T(8,128)(2,1)S(1)}, u32[]{:S(2)}, u32[]{:S(2)}) collective-permute-start(bf16[2,9,32,128]{3,2,1,0:T(8,128)(2,1)S(1)} %collective-permute-done.33.refs_6_), channel_id=1, source_target_pairs={{0,1},{1,0},{2,3},{3,2},{4,5},{5,4},{6,7},{7,6},{8,9},{9,8},{10,11... | collective-permute-start | bytes 442376 | tf_op jit(solution)/shard_map/ppermute | solution.py:274
  92.6 1.5 %collective-permute-start.42 = (bf16[2,9,32,128]{3,2,1,0:T(8,128)(2,1)S(1)}, bf16[2,9,32,128]{3,2,1,0:T(8,128)(2,1)S(1)}, u32[]{:S(2)}, u32[]{:S(2)}) collective-permute-start(bf16[2,9,32,128]{3,2,1,0:T(8,128)(2,1)S(1)} %collective-permute-done.34.refs_7_), channel_id=1, source_target_pairs={{0,1},{1,0},{2,3},{3,2},{4,5},{5,4},{6,7},{7,6},{8,9},{9,8},{10,11... | collective-permute-start | bytes 442376 | tf_op jit(solution)/shard_map/ppermute | solution.py:274
  97.6 2.1 %collective-permute-start.43 = (bf16[4,2,9,32,128]{4,3,2,1,0:T(8,128)(2,1)S(1)}, bf16[4,2,9,32,128]{4,3,2,1,0:T(8,128)(2,1)S(1)}, u32[]{:S(2)}, u32[]{:S(2)}) collective-permute-start(bf16[4,2,9,32,128]{4,3,2,1,0:T(8,128)(2,1)S(1)} %get-tuple-element.186), channel_id=1, source_target_pairs={{0,1},{1,0},{2,3},{3,2},{4,5},{5,4},{6,7},{7,6},{8,9},{9,8},{10,11... | collective-permute-start | bytes 1769480 | tf_op jit(solution)/shard_map/ppermute | solution.py:274
  99.8 11.2 %collective-permute-start.48 = (bf16[4,2,9,32,128]{4,3,2,1,0:T(8,128)(2,1)S(1)}, bf16[4,2,9,32,128]{4,3,2,1,0:T(8,128)(2,1)S(1)}, u32[]{:S(2)}, u32[]{:S(2)}) collective-permute-start(bf16[4,2,9,32,128]{4,3,2,1,0:T(8,128)(2,1)S(1)} %get-tuple-element.196), channel_id=1, source_target_pairs={{0,1},{1,0},{2,3},{3,2},{4,5},{5,4},{6,7},{7,6},{8,9},{9,8},{10,11... | collective-permute-start | bytes 1769480 | tf_op jit(solution)/shard_map/ppermute | solution.py:274
  100.1 5.5 %collective-permute-start.44 = (bf16[2,9,32,128]{3,2,1,0:T(8,128)(2,1)S(1)}, bf16[2,9,32,128]{3,2,1,0:T(8,128)(2,1)S(1)}, u32[]{:S(2)}, u32[]{:S(2)}) collective-permute-start(bf16[2,9,32,128]{3,2,1,0:T(8,128)(2,1)S(1)} %get-tuple-element.192), channel_id=1, source_target_pairs={{0,4},{1,9},{2,6},{3,11},{4,0},{5,13},{6,2},{7,15},{8,12},{9,1},{1... | collective-permute-start | bytes 442376 | tf_op jit(solution)/shard_map/ppermute | solution.py:269
  102.2 5.8 %collective-permute-start.45 = (bf16[2,9,32,128]{3,2,1,0:T(8,128)(2,1)S(1)}, bf16[2,9,32,128]{3,2,1,0:T(8,128)(2,1)S(1)}, u32[]{:S(2)}, u32[]{:S(2)}) collective-permute-start(bf16[2,9,32,128]{3,2,1,0:T(8,128)(2,1)S(1)} %get-tuple-element.193), channel_id=1, source_target_pairs={{0,8},{1,3},{2,10},{3,1},{4,12},{5,7},{6,14},{7,5},{8,0},{9,11},{1... | collective-permute-start | bytes 442376 | tf_op jit(solution)/shard_map/ppermute | solution.py:269
  102.9 6.1 %collective-permute-start.46 = (bf16[2,9,32,128]{3,2,1,0:T(8,128)(2,1)S(1)}, bf16[2,9,32,128]{3,2,1,0:T(8,128)(2,1)S(1)}, u32[]{:S(2)}, u32[]{:S(2)}) collective-permute-start(bf16[2,9,32,128]{3,2,1,0:T(8,128)(2,1)S(1)} %get-tuple-element.194), channel_id=1, source_target_pairs={{0,2},{1,5},{2,0},{3,7},{4,6},{5,1},{6,4},{7,3},{8,10},{9,13},{10,... | collective-permute-start | bytes 442376 | tf_op jit(solution)/shard_map/ppermute | solution.py:269
  104.9 6.0 %collective-permute-start.47 = (bf16[2,9,32,128]{3,2,1,0:T(8,128)(2,1)S(1)}, bf16[2,9,32,128]{3,2,1,0:T(8,128)(2,1)S(1)}, u32[]{:S(2)}, u32[]{:S(2)}) collective-permute-start(bf16[2,9,32,128]{3,2,1,0:T(8,128)(2,1)S(1)} %get-tuple-element.195), channel_id=1, source_target_pairs={{0,12},{1,11},{2,14},{3,9},{4,8},{5,15},{6,10},{7,13},{8,4},{9,3},... | collective-permute-start | bytes 442376 | tf_op jit(solution)/shard_map/ppermute | solution.py:269
  111.2 6.5 %collective-permute-start.49 = (bf16[2,9,32,128]{3,2,1,0:T(8,128)(2,1)S(1)}, bf16[2,9,32,128]{3,2,1,0:T(8,128)(2,1)S(1)}, u32[]{:S(2)}, u32[]{:S(2)}) collective-permute-start(bf16[2,9,32,128]{3,2,1,0:T(8,128)(2,1)S(1)} %get-tuple-element.209), channel_id=1, source_target_pairs={{0,2},{1,5},{2,0},{3,7},{4,6},{5,1},{6,4},{7,3},{8,10},{9,13},{10,... | collective-permute-start | bytes 442376 | tf_op jit(solution)/shard_map/ppermute | solution.py:269
  113.0 5.1 %collective-permute-start.50 = (bf16[2,9,32,128]{3,2,1,0:T(8,128)(2,1)S(1)}, bf16[2,9,32,128]{3,2,1,0:T(8,128)(2,1)S(1)}, u32[]{:S(2)}, u32[]{:S(2)}) collective-permute-start(bf16[2,9,32,128]{3,2,1,0:T(8,128)(2,1)S(1)} %get-tuple-element.210), channel_id=1, source_target_pairs={{0,4},{1,9},{2,6},{3,11},{4,0},{5,13},{6,2},{7,15},{8,12},{9,1},{1... | collective-permute-start | bytes 442376 | tf_op jit(solution)/shard_map/ppermute | solution.py:269
  114.2 5.1 %collective-permute-start.51 = (bf16[2,9,32,128]{3,2,1,0:T(8,128)(2,1)S(1)}, bf16[2,9,32,128]{3,2,1,0:T(8,128)(2,1)S(1)}, u32[]{:S(2)}, u32[]{:S(2)}) collective-permute-start(bf16[2,9,32,128]{3,2,1,0:T(8,128)(2,1)S(1)} %get-tuple-element.211), channel_id=1, source_target_pairs={{0,8},{1,3},{2,10},{3,1},{4,12},{5,7},{6,14},{7,5},{8,0},{9,11},{1... | collective-permute-start | bytes 442376 | tf_op jit(solution)/shard_map/ppermute | solution.py:269
  119.4 6.1 %collective-permute-start.52 = (bf16[9,32,128]{2,1,0:T(8,128)(2,1)S(1)}, bf16[9,32,128]{2,1,0:T(8,128)(2,1)S(1)}, u32[]{:S(2)}, u32[]{:S(2)}) collective-permute-start(bf16[9,32,128]{2,1,0:T(8,128)(2,1)S(1)} %get-tuple-element.218), channel_id=1, source_target_pairs={{0,16},{1,17},{2,18},{3,19},{4,20},{5,21},{6,22},{7,23},{8,24},{9,... | collective-permute-start | bytes 221192 | tf_op jit(solution)/shard_map/ppermute | solution.py:265
  121.1 1.2 collective-permute-start.53
  121.1 1.3 %collective-permute-start.54 = (bf16[1,32,256]{2,1,0:T(8,128)(2,1)S(1)}, bf16[1,32,256]{2,1,0:T(8,128)(2,1)S(1)}, u32[]{:S(2)}, u32[]{:S(2)}) collective-permute-start(bf16[1,32,256]{2,1,0:T(8,128)(2,1)S(1)} %collective-permute-done.27), channel_id=1, source_target_pairs={{0,1},{1,0},{2,3},{3,2},{4,5},{5,4},{6,7},{7,6},{8,9},{9,8},{10,11... | collective-permute-start | bytes 49160 | tf_op jit(solution)/shard_map/ppermute | solution.py:274
  (3 other events, 13.1 us)

commit v25 on v22

--- a/solution.py
+++ b/solution.py
@@ -120,7 +120,7 @@
                 total[row + c] = jnp.zeros((rhs, LANES), F32)
         return 0
 
-    lax.fori_loop(0, far, split, 0)
+    lax.fori_loop(0, far, split, 0, unroll=far <= 2)
 
     def some(s, _):
         for u in range(unroll):
@@ -143,7 +143,7 @@
                             out_refs[core * len(order) + g][place, f, 3 * q + k] = tile.astype(BF)
         return 0
 
-    lax.fori_loop(0, far, pack, 0)
+    lax.fori_loop(0, far, pack, 0, unroll=far <= 2)
 
 
 def order_kernel(_, __, out_ref):

time: 125 us -> 125 us (level)
  no operation moved by 1% of the time
where the time goes in v25:
time: 125 us; the launch traced here: 124 us
  starting transfers between devices  53 us (42%)
  waiting for transfers between devices  49.4 us (40%)
  Pallas kernels  15.5 us (12%)
  local copies, waits for them, and re-layouts  5.66 us (5%)
    ppermute x28, starting transfers between devices, swap(): lax.ppermute(part, 'clu', [(d, d ^ (turned if d % cores else direction) *...  36.9 us
    ppermute x28, waiting for transfers between devices, swap(): lax.ppermute(part, 'clu', [(d, d ^ (turned if d % cores else direction) *...  27.1 us
    ppermute x4, waiting for transfers between devices, swap_far(): lax.ppermute(part, 'clu', [(d, (d + shift * cube) % devices) for d in ran...  10.4 us
    ppermute x4, starting transfers between devices, swap_far(): lax.ppermute(part, 'clu', [(d, (d + shift * cube) % devices) for d in ran...  8.39 us
    ppermute x21, waiting for transfers between devices, swap_cores(): return lax.ppermute(part, 'clu', [(d, d ^ 1) for d in range(devices)])  7.59 us
    pallas_call x2, Pallas kernels, couple(): pl.pallas_call(functools.partial(couple_kernel, order=order, joined=joine...  6.47 us
    unnamed x25, local copies, waits for them, and re-layouts  5.66 us
    ppermute x21, starting transfers between devices, swap_cores(): return lax.ppermute(part, 'clu', [(d, d ^ 1) for d in range(devices)])  4.98 us
  transfers between devices with their start and end apart: 55, of which 39 were waited for; matrix products, arithmetic and copies ran while one was open for 4% of the time, Pallas kernels for 2%

profile of v25, /device:TPU:0, one launch (start us, length us, event | category | flops | bytes accessed | tf_op | source)
XLA Modules:
  0.0 124.4 jit_solution(15438439567517129747)
XLA Ops:
  0.6 2.9 %shard_map.95 = (bf16[9,32,128]{2,1,0:T(8,128)(2,1)}, bf16[1,32,256]{2,1,0:T(8,128)(2,1)}, bf16[1,32,256]{2,1,0:T(8,128)(2,1)}) custom-call(s32[12]{0:T(128)} %ranks_ref.5, bf16[8,32,256]{2,1,0:T(8,128)(2,1)} %v_ref.1, bf16[8,96,256]{2,1,0:T(8,128)(2,1)} %basis_ref.3, bf16[8,96,96]{2,1,0:T(8,128)(2,1)} %transfer_ref.3), custom_call_target="tpu_custom_call" | custom-call | tf_op jit(solution)/shard_map/pallas_call | solution.py:297
  3.6 4.1 %collective-permute-start = (bf16[9,32,128]{2,1,0:T(8,128)(2,1)}, bf16[9,32,128]{2,1,0:T(8,128)(2,1)S(1)}, u32[]{:S(2)}, u32[]{:S(2)}) collective-permute-start(bf16[9,32,128]{2,1,0:T(8,128)(2,1)} %get-tuple-element.112.__.refs_0_), channel_id=1, source_target_pairs={{0,16},{1,17},{2,18},{3,19},{4,20},{5,21},{6,22},{7,23},{8,24},{9,... | collective-permute-start | bytes 221192 | tf_op jit(solution)/shard_map/ppermute | solution.py:265
  7.7 4.8 %copy.10._.coupling_ref = bf16[128,96,96]{2,1,0:T(8,128)(2,1)} copy(bf16[128,96,96]{0,2,1:T(8,128)(2,1)} %param.12) | data formatting | bytes 4718592 | tf_op args[4]
  12.5 0.6 shard_map.96._
  13.0 0.8 copy-done.6
  13.9 1.6 %collective-permute-start.3 = (bf16[2,9,32,128]{3,2,1,0:T(8,128)(2,1)S(1)}, bf16[2,9,32,128]{3,2,1,0:T(8,128)(2,1)S(1)}, u32[]{:S(2)}, u32[]{:S(2)}) collective-permute-start(bf16[2,9,32,128]{3,2,1,0:T(8,128)(2,1)S(1)} %shard_map.97.refs_0_), channel_id=1, source_target_pairs={{0,8},{1,3},{2,10},{3,1},{4,12},{5,7},{6,14},{7,5},{8,0},{9,11},{1... | collective-permute-start | bytes 442376 | tf_op jit(solution)/shard_map/ppermute | solution.py:269
  15.5 1.5 %collective-permute-start.2 = (bf16[2,9,32,128]{3,2,1,0:T(8,128)(2,1)S(1)}, bf16[2,9,32,128]{3,2,1,0:T(8,128)(2,1)S(1)}, u32[]{:S(2)}, u32[]{:S(2)}) collective-permute-start(bf16[2,9,32,128]{3,2,1,0:T(8,128)(2,1)S(1)} %shard_map.97.refs_0_), channel_id=1, source_target_pairs={{0,4},{1,9},{2,6},{3,11},{4,0},{5,13},{6,2},{7,15},{8,12},{9,1},{1... | collective-permute-start | bytes 442376 | tf_op jit(solution)/shard_map/ppermute | solution.py:269
  17.0 1.5 %collective-permute-start.1 = (bf16[2,9,32,128]{3,2,1,0:T(8,128)(2,1)S(1)}, bf16[2,9,32,128]{3,2,1,0:T(8,128)(2,1)S(1)}, u32[]{:S(2)}, u32[]{:S(2)}) collective-permute-start(bf16[2,9,32,128]{3,2,1,0:T(8,128)(2,1)S(1)} %shard_map.97.refs_0_), channel_id=1, source_target_pairs={{0,2},{1,5},{2,0},{3,7},{4,6},{5,1},{6,4},{7,3},{8,10},{9,13},{10,... | collective-permute-start | bytes 442376 | tf_op jit(solution)/shard_map/ppermute | solution.py:269
  18.5 0.6 shard_map.98.near_ref
  19.1 1.3 %collective-permute-done.3.refs_3_ = bf16[2,9,32,128]{3,2,1,0:T(8,128)(2,1)S(1)} collective-permute-done((bf16[2,9,32,128]{3,2,1,0:T(8,128)(2,1)S(1)}, bf16[2,9,32,128]{3,2,1,0:T(8,128)(2,1)S(1)}, u32[]{:S(2)}, u32[]{:S(2)}) %collective-permute-start.3) | collective-permute-done | bytes 147488 | tf_op jit(solution)/shard_map/ppermute | solution.py:269
  20.5 1.3 %collective-permute-done.2.refs_2_ = bf16[2,9,32,128]{3,2,1,0:T(8,128)(2,1)S(1)} collective-permute-done((bf16[2,9,32,128]{3,2,1,0:T(8,128)(2,1)S(1)}, bf16[2,9,32,128]{3,2,1,0:T(8,128)(2,1)S(1)}, u32[]{:S(2)}, u32[]{:S(2)}) %collective-permute-start.2) | collective-permute-done | bytes 147488 | tf_op jit(solution)/shard_map/ppermute | solution.py:269
  22.3 0.5 collective-permute-start.6
  22.8 1.5 %collective-permute-start.7 = (bf16[2,9,32,128]{3,2,1,0:T(8,128)(2,1)S(1)}, bf16[2,9,32,128]{3,2,1,0:T(8,128)(2,1)S(1)}, u32[]{:S(2)}, u32[]{:S(2)}) collective-permute-start(bf16[2,9,32,128]{3,2,1,0:T(8,128)(2,1)S(1)} %collective-permute-done.3.refs_3_), channel_id=1, source_target_pairs={{0,2},{1,5},{2,0},{3,7},{4,6},{5,1},{6,4},{7,3},{8,10},{9,13},{10,... | collective-permute-start | bytes 442376 | tf_op jit(solution)/shard_map/ppermute | solution.py:269
  24.8 2.5 %collective-permute-start.4 = (bf16[2,9,32,128]{3,2,1,0:T(8,128)(2,1)S(1)}, bf16[2,9,32,128]{3,2,1,0:T(8,128)(2,1)S(1)}, u32[]{:S(2)}, u32[]{:S(2)}) collective-permute-start(bf16[2,9,32,128]{3,2,1,0:T(8,128)(2,1)S(1)} %collective-permute-done.1.refs_1_), channel_id=1, source_target_pairs={{0,12},{1,11},{2,14},{3,9},{4,8},{5,15},{6,10},{7,13},{8,4},{9,3},... | collective-permute-start | bytes 442376 | tf_op jit(solution)/shard_map/ppermute | solution.py:269
  27.3 0.9 collective-permute-done.6.refs_3_
  28.6 1.6 %collective-permute-done.5.refs_2_ = bf16[2,9,32,128]{3,2,1,0:T(8,128)(2,1)S(1)} collective-permute-done((bf16[2,9,32,128]{3,2,1,0:T(8,128)(2,1)S(1)}, bf16[2,9,32,128]{3,2,1,0:T(8,128)(2,1)S(1)}, u32[]{:S(2)}, u32[]{:S(2)}) %collective-permute-start.5) | collective-permute-done | bytes 147488 | tf_op jit(solution)/shard_map/ppermute | solution.py:269
  30.2 2.3 %collective-permute-done.4.refs_1_ = bf16[2,9,32,128]{3,2,1,0:T(8,128)(2,1)S(1)} collective-permute-done((bf16[2,9,32,128]{3,2,1,0:T(8,128)(2,1)S(1)}, bf16[2,9,32,128]{3,2,1,0:T(8,128)(2,1)S(1)}, u32[]{:S(2)}, u32[]{:S(2)}) %collective-permute-start.4) | collective-permute-done | bytes 147488 | tf_op jit(solution)/shard_map/ppermute | solution.py:269
  34.9 3.2 %shard_map.101 = (bf16[4,2,9,32,128]{4,3,2,1,0:T(8,128)(2,1)S(1)}, bf16[4,2,9,32,128]{4,3,2,1,0:T(8,128)(2,1)S(1)}, bf16[4,2,9,32,128]{4,3,2,1,0:T(8,128)(2,1)S(1)}, bf16[4,2,9,32,128]{4,3,2,1,0:T(8,128)(2,1)S(1)}) custom-call(s32[128]{0:T(128)S(1)} %bitcast.4, s32[128]{0:T(128)S(1)} %bitcast.6, bf16[128,96,96]{2,1,0:T(8,128)(2,1)S(1)} %copy-done.1, ...), custom_call_target="tpu_custom_call" | custom-call | flops 75497472 | bytes 10485760 | tf_op jit(solution)/shard_map/pallas_call | solution.py:312
  38.4 1.8 %collective-permute-done.13.swap_ref = bf16[4,2,9,32,128]{4,3,2,1,0:T(8,128)(2,1)S(1)} collective-permute-done((bf16[4,2,9,32,128]{4,3,2,1,0:T(8,128)(2,1)S(1)}, bf16[4,2,9,32,128]{4,3,2,1,0:T(8,128)(2,1)S(1)}, u32[]{:S(2)}, u32[]{:S(2)}) %collective-permute-start.13) | collective-permute-done | bytes 589856 | tf_op jit(solution)/shard_map/ppermute | solution.py:274
  40.6 1.0 collective-permute-start.14
  42.1 1.5 %collective-permute-start.16 = (bf16[2,9,32,128]{3,2,1,0:T(8,128)(2,1)S(1)}, bf16[2,9,32,128]{3,2,1,0:T(8,128)(2,1)S(1)}, u32[]{:S(2)}, u32[]{:S(2)}) collective-permute-start(bf16[2,9,32,128]{3,2,1,0:T(8,128)(2,1)S(1)} %get-tuple-element.135), channel_id=1, source_target_pairs={{0,2},{1,5},{2,0},{3,7},{4,6},{5,1},{6,4},{7,3},{8,10},{9,13},{10,... | collective-permute-start | bytes 442376 | tf_op jit(solution)/shard_map/ppermute | solution.py:269
  43.6 2.0 %collective-permute-start.21 = (bf16[2,9,32,128]{3,2,1,0:T(8,128)(2,1)S(1)}, bf16[2,9,32,128]{3,2,1,0:T(8,128)(2,1)S(1)}, u32[]{:S(2)}, u32[]{:S(2)}) collective-permute-start(bf16[2,9,32,128]{3,2,1,0:T(8,128)(2,1)S(1)} %get-tuple-element.151), channel_id=1, source_target_pairs={{0,14},{1,15},{2,12},{3,13},{4,10},{5,11},{6,8},{7,9},{8,6},{9,7},... | collective-permute-start | bytes 442376 | tf_op jit(solution)/shard_map/ppermute | solution.py:269
  45.6 1.6 %collective-permute-done.14.refs_0_ = bf16[2,9,32,128]{3,2,1,0:T(8,128)(2,1)S(1)} collective-permute-done((bf16[2,9,32,128]{3,2,1,0:T(8,128)(2,1)S(1)}, bf16[2,9,32,128]{3,2,1,0:T(8,128)(2,1)S(1)}, u32[]{:S(2)}, u32[]{:S(2)}) %collective-permute-start.14) | collective-permute-done | bytes 147488 | tf_op jit(solution)/shard_map/ppermute | solution.py:269
  47.5 1.9 %collective-permute-done.16.refs_2_ = bf16[2,9,32,128]{3,2,1,0:T(8,128)(2,1)S(1)} collective-permute-done((bf16[2,9,32,128]{3,2,1,0:T(8,128)(2,1)S(1)}, bf16[2,9,32,128]{3,2,1,0:T(8,128)(2,1)S(1)}, u32[]{:S(2)}, u32[]{:S(2)}) %collective-permute-start.16) | collective-permute-done | bytes 147488 | tf_op jit(solution)/shard_map/ppermute | solution.py:269
  49.6 2.5 %collective-permute-start.18 = (bf16[2,9,32,128]{3,2,1,0:T(8,128)(2,1)S(1)}, bf16[2,9,32,128]{3,2,1,0:T(8,128)(2,1)S(1)}, u32[]{:S(2)}, u32[]{:S(2)}) collective-permute-start(bf16[2,9,32,128]{3,2,1,0:T(8,128)(2,1)S(1)} %get-tuple-element.148), channel_id=1, source_target_pairs={{0,2},{1,5},{2,0},{3,7},{4,6},{5,1},{6,4},{7,3},{8,10},{9,13},{10,... | collective-permute-start | bytes 442376 | tf_op jit(solution)/shard_map/ppermute | solution.py:269
  52.1 2.0 %collective-permute-start.20 = (bf16[2,9,32,128]{3,2,1,0:T(8,128)(2,1)S(1)}, bf16[2,9,32,128]{3,2,1,0:T(8,128)(2,1)S(1)}, u32[]{:S(2)}, u32[]{:S(2)}) collective-permute-start(bf16[2,9,32,128]{3,2,1,0:T(8,128)(2,1)S(1)} %get-tuple-element.150), channel_id=1, source_target_pairs={{0,8},{1,3},{2,10},{3,1},{4,12},{5,7},{6,14},{7,5},{8,0},{9,11},{1... | collective-permute-start | bytes 442376 | tf_op jit(solution)/shard_map/ppermute | solution.py:269
  54.2 1.3 %collective-permute-start.22 = (bf16[1,32,256]{2,1,0:T(8,128)(2,1)S(1)}, bf16[1,32,256]{2,1,0:T(8,128)(2,1)S(1)}, u32[]{:S(2)}, u32[]{:S(2)}) collective-permute-start(bf16[1,32,256]{2,1,0:T(8,128)(2,1)S(1)} %copy-done.11), channel_id=1, source_target_pairs={{1,3},{3,5},{5,7},{7,9},{9,11},{11,13},{13,15},{15,17},{17,19},{19... | collective-permute-start | bytes 49160 | tf_op jit(solution)/shard_map/ppermute | solution.py:432
  55.5 4.3 %collective-permute-done.22 = bf16[1,32,256]{2,1,0:T(8,128)(2,1)S(1)} collective-permute-done((bf16[1,32,256]{2,1,0:T(8,128)(2,1)S(1)}, bf16[1,32,256]{2,1,0:T(8,128)(2,1)S(1)}, u32[]{:S(2)}, u32[]{:S(2)}) %collective-permute-start.22) | collective-permute-done | bytes 16416 | tf_op jit(solution)/shard_map/ppermute | solution.py:432
  59.9 1.2 collective-permute-start.23
  61.6 0.7 collective-permute-done.24.inner_ref
  62.6 3.4 %collective-permute-done.23.rest_0_ = bf16[9,32,128]{2,1,0:T(8,128)(2,1)S(1)} collective-permute-done((bf16[9,32,128]{2,1,0:T(8,128)(2,1)S(1)}, bf16[9,32,128]{2,1,0:T(8,128)(2,1)S(1)}, u32[]{:S(2)}, u32[]{:S(2)}) %collective-permute-start.23) | collective-permute-done | bytes 73760 | tf_op jit(solution)/shard_map/ppermute | solution.py:265
  66.1 1.6 %shard_map.106 = (bf16[8,32,256]{2,1,0:T(8,128)(2,1)}, bf16[9,32,128]{2,1,0:T(8,128)(2,1)S(1)}, bf16[1,32,256]{2,1,0:T(8,128)(2,1)S(1)}, bf16[1,32,256]{2,1,0:T(8,128)(2,1)S(1)}, bf16[8,32,256]{2,1,0:T(8,128)(2,1)S(1)}) custom-call(s32[12]{0:T(128)S(1)} %copy-done.7, f32[8,32,256]{2,1,0:T(8,128)S(1)} %shard_map.98.near_ref, ...), custom_call_target="tpu_custom_call" | custom-call | tf_op jit(solution)/shard_map/pallas_call | solution.py:438
  68.1 5.1 %collective-permute-done.26.refs_1_ = bf16[9,32,128]{2,1,0:T(8,128)(2,1)S(1)} collective-permute-done((bf16[9,32,128]{2,1,0:T(8,128)(2,1)S(1)}, bf16[9,32,128]{2,1,0:T(8,128)(2,1)S(1)}, u32[]{:S(2)}, u32[]{:S(2)}) %collective-permute-start.26) | collective-permute-done | bytes 73760 | tf_op jit(solution)/shard_map/ppermute | solution.py:265
  73.3 1.4 %collective-permute-start.28 = (bf16[2,9,32,128]{3,2,1,0:T(8,128)(2,1)S(1)}, bf16[2,9,32,128]{3,2,1,0:T(8,128)(2,1)S(1)}, u32[]{:S(2)}, u32[]{:S(2)}) collective-permute-start(bf16[2,9,32,128]{3,2,1,0:T(8,128)(2,1)S(1)} %shard_map.107.refs_0_), channel_id=1, source_target_pairs={{0,4},{1,9},{2,6},{3,11},{4,0},{5,13},{6,2},{7,15},{8,12},{9,1},{1... | collective-permute-start | bytes 442376 | tf_op jit(solution)/shard_map/ppermute | solution.py:269
  74.6 1.9 %collective-permute-start.27 = (bf16[2,9,32,128]{3,2,1,0:T(8,128)(2,1)S(1)}, bf16[2,9,32,128]{3,2,1,0:T(8,128)(2,1)S(1)}, u32[]{:S(2)}, u32[]{:S(2)}) collective-permute-start(bf16[2,9,32,128]{3,2,1,0:T(8,128)(2,1)S(1)} %shard_map.107.refs_0_), channel_id=1, source_target_pairs={{0,2},{1,5},{2,0},{3,7},{4,6},{5,1},{6,4},{7,3},{8,10},{9,13},{10,... | collective-permute-start | bytes 442376 | tf_op jit(solution)/shard_map/ppermute | solution.py:269
  76.5 0.6 shard_map.108.near_ref
  77.1 1.7 %collective-permute-start.33 = (bf16[2,9,32,128]{3,2,1,0:T(8,128)(2,1)S(1)}, bf16[2,9,32,128]{3,2,1,0:T(8,128)(2,1)S(1)}, u32[]{:S(2)}, u32[]{:S(2)}) collective-permute-start(bf16[2,9,32,128]{3,2,1,0:T(8,128)(2,1)S(1)} %shard_map.107.refs_0_), channel_id=1, source_target_pairs={{0,14},{1,15},{2,12},{3,13},{4,10},{5,11},{6,8},{7,9},{8,6},{9,7},... | collective-permute-start | bytes 442376 | tf_op jit(solution)/shard_map/ppermute | solution.py:269
  78.8 0.9 collective-permute-done.29.refs_4_
  80.0 1.1 collective-permute-start.30
  81.1 1.5 %collective-permute-start.34 = (bf16[1,32,256]{2,1,0:T(8,128)(2,1)S(1)}, bf16[1,32,256]{2,1,0:T(8,128)(2,1)S(1)}, u32[]{:S(2)}, u32[]{:S(2)}) collective-permute-start(bf16[1,32,256]{2,1,0:T(8,128)(2,1)S(1)} %get-tuple-element.173), channel_id=1, source_target_pairs={{1,3},{3,5},{5,7},{7,9},{9,11},{11,13},{13,15},{15,17},{17,19},{19... | collective-permute-start | bytes 49160 | tf_op jit(solution)/shard_map/ppermute | solution.py:416
  82.6 4.4 %collective-permute-start.32 = (bf16[2,9,32,128]{3,2,1,0:T(8,128)(2,1)S(1)}, bf16[2,9,32,128]{3,2,1,0:T(8,128)(2,1)S(1)}, u32[]{:S(2)}, u32[]{:S(2)}) collective-permute-start(bf16[2,9,32,128]{3,2,1,0:T(8,128)(2,1)S(1)} %collective-permute-done.28.refs_2_), channel_id=1, source_target_pairs={{0,8},{1,3},{2,10},{3,1},{4,12},{5,7},{6,14},{7,5},{8,0},{9,11},{1... | collective-permute-start | bytes 442376 | tf_op jit(solution)/shard_map/ppermute | solution.py:269
  86.9 0.7 collective-permute-start.31
  88.2 1.9 %collective-permute-done.32.refs_6_ = bf16[2,9,32,128]{3,2,1,0:T(8,128)(2,1)S(1)} collective-permute-done((bf16[2,9,32,128]{3,2,1,0:T(8,128)(2,1)S(1)}, bf16[2,9,32,128]{3,2,1,0:T(8,128)(2,1)S(1)}, u32[]{:S(2)}, u32[]{:S(2)}) %collective-permute-start.32) | collective-permute-done | bytes 147488 | tf_op jit(solution)/shard_map/ppermute | solution.py:269
  90.1 2.0 %collective-permute-done.31.refs_5_ = bf16[2,9,32,128]{3,2,1,0:T(8,128)(2,1)S(1)} collective-permute-done((bf16[2,9,32,128]{3,2,1,0:T(8,128)(2,1)S(1)}, bf16[2,9,32,128]{3,2,1,0:T(8,128)(2,1)S(1)}, u32[]{:S(2)}, u32[]{:S(2)}) %collective-permute-start.31) | collective-permute-done | bytes 147488 | tf_op jit(solution)/shard_map/ppermute | solution.py:269
  92.1 0.5 collective-permute-start.40
  94.2 3.2 %shard_map.109 = (bf16[4,2,9,32,128]{4,3,2,1,0:T(8,128)(2,1)S(1)}, bf16[4,2,9,32,128]{4,3,2,1,0:T(8,128)(2,1)S(1)}, bf16[4,2,9,32,128]{4,3,2,1,0:T(8,128)(2,1)S(1)}, bf16[4,2,9,32,128]{4,3,2,1,0:T(8,128)(2,1)S(1)}) custom-call(s32[128]{0:T(128)S(1)} %bitcast.5, s32[128]{0:T(128)S(1)} %bitcast.7, bf16[128,96,96]{2,1,0:T(8,128)(2,1)S(1)} %copy-done.1, ...), custom_call_target="tpu_custom_call" | custom-call | flops 75497472 | bytes 10485760 | tf_op jit(solution)/shard_map/pallas_call | solution.py:312
  97.8 1.7 %collective-permute-done.43.swap_ref = bf16[4,2,9,32,128]{4,3,2,1,0:T(8,128)(2,1)S(1)} collective-permute-done((bf16[4,2,9,32,128]{4,3,2,1,0:T(8,128)(2,1)S(1)}, bf16[4,2,9,32,128]{4,3,2,1,0:T(8,128)(2,1)S(1)}, u32[]{:S(2)}, u32[]{:S(2)}) %collective-permute-start.43) | collective-permute-done | bytes 589856 | tf_op jit(solution)/shard_map/ppermute | solution.py:274
  100.0 1.2 collective-permute-start.44
  101.2 0.6 collective-permute-start.45
  101.8 0.5 collective-permute-start.46
  102.3 1.9 %collective-permute-start.47 = (bf16[2,9,32,128]{3,2,1,0:T(8,128)(2,1)S(1)}, bf16[2,9,32,128]{3,2,1,0:T(8,128)(2,1)S(1)}, u32[]{:S(2)}, u32[]{:S(2)}) collective-permute-start(bf16[2,9,32,128]{3,2,1,0:T(8,128)(2,1)S(1)} %get-tuple-element.193), channel_id=1, source_target_pairs={{0,12},{1,11},{2,14},{3,9},{4,8},{5,15},{6,10},{7,13},{8,4},{9,3},... | collective-permute-start | bytes 442376 | tf_op jit(solution)/shard_map/ppermute | solution.py:269
  104.2 2.2 %collective-permute-done.44.refs_0_ = bf16[2,9,32,128]{3,2,1,0:T(8,128)(2,1)S(1)} collective-permute-done((bf16[2,9,32,128]{3,2,1,0:T(8,128)(2,1)S(1)}, bf16[2,9,32,128]{3,2,1,0:T(8,128)(2,1)S(1)}, u32[]{:S(2)}, u32[]{:S(2)}) %collective-permute-start.44) | collective-permute-done | bytes 147488 | tf_op jit(solution)/shard_map/ppermute | solution.py:269
  106.4 1.1 collective-permute-done.45.refs_1_
  107.5 0.9 collective-permute-done.46.refs_2_
  108.5 1.3 %collective-permute-done.47.refs_3_ = bf16[2,9,32,128]{3,2,1,0:T(8,128)(2,1)S(1)} collective-permute-done((bf16[2,9,32,128]{3,2,1,0:T(8,128)(2,1)S(1)}, bf16[2,9,32,128]{3,2,1,0:T(8,128)(2,1)S(1)}, u32[]{:S(2)}, u32[]{:S(2)}) %collective-permute-start.47) | collective-permute-done | bytes 147488 | tf_op jit(solution)/shard_map/ppermute | solution.py:269
  110.0 0.7 collective-permute-start.49
  110.7 0.8 collective-permute-start.50
  111.5 0.9 collective-permute-start.51
  112.4 3.1 %collective-permute-done.49.refs_0_ = bf16[2,9,32,128]{3,2,1,0:T(8,128)(2,1)S(1)} collective-permute-done((bf16[2,9,32,128]{3,2,1,0:T(8,128)(2,1)S(1)}, bf16[2,9,32,128]{3,2,1,0:T(8,128)(2,1)S(1)}, u32[]{:S(2)}, u32[]{:S(2)}) %collective-permute-start.49) | collective-permute-done | bytes 147488 | tf_op jit(solution)/shard_map/ppermute | solution.py:269
  115.9 0.8 collective-permute-done.51.refs_2_
  116.8 2.7 %collective-permute-start.52 = (bf16[9,32,128]{2,1,0:T(8,128)(2,1)S(1)}, bf16[9,32,128]{2,1,0:T(8,128)(2,1)S(1)}, u32[]{:S(2)}, u32[]{:S(2)}) collective-permute-start(bf16[9,32,128]{2,1,0:T(8,128)(2,1)S(1)} %get-tuple-element.216), channel_id=1, source_target_pairs={{0,16},{1,17},{2,18},{3,19},{4,20},{5,21},{6,22},{7,23},{8,24},{9,... | collective-permute-start | bytes 221192 | tf_op jit(solution)/shard_map/ppermute | solution.py:265
  119.9 0.7 collective-permute-done.53.inner_ref
  120.9 1.9 %collective-permute-done.52.rest_0_ = bf16[9,32,128]{2,1,0:T(8,128)(2,1)S(1)} collective-permute-done((bf16[9,32,128]{2,1,0:T(8,128)(2,1)S(1)}, bf16[9,32,128]{2,1,0:T(8,128)(2,1)S(1)}, u32[]{:S(2)}, u32[]{:S(2)}) %collective-permute-start.52) | collective-permute-done | bytes 73760 | tf_op jit(solution)/shard_map/ppermute | solution.py:265
  122.9 1.6 %shard_map.114 = bf16[8,32,256]{2,1,0:T(8,128)(2,1)} custom-call(s32[12]{0:T(128)S(1)} %copy-done.7, f32[8,32,256]{2,1,0:T(8,128)S(1)} %shard_map.108.near_ref, f32[2,32,256]{2,1,0:T(8,128)S(1)} %shard_map.113.edge_ref, bf16[8,96,256]{2,1,0:T(8,128)(2,1)S(1)} %copy-done.2, bf16[8,96,96]{2,1,0:T(8,128)(2,1)S(1)} %copy-done.3, ...), custom_call_target="tpu_custom_call" | custom-call | tf_op jit(solution)/shard_map/pallas_call | solution.py:438
  (91 shorter events, 11.8 us)
Async XLA Ops:
  3.5 9.5 %copy-start.5 = (bf16[9,32,128]{2,1,0:T(8,128)(2,1)S(1)}, bf16[9,32,128]{2,1,0:T(8,128)(2,1)}, u32[]{:S(2)}) copy-start(bf16[9,32,128]{2,1,0:T(8,128)(2,1)} %get-tuple-element.112.__.refs_0_) | copy-start | bytes 221188
  3.5 15.0 %copy-start = (bf16[8,3,256,256]{3,2,1,0:T(8,128)(2,1)S(1)}, bf16[8,3,256,256]{3,2,1,0:T(8,128)(2,1)}, u32[]{:S(2)}) copy-start(bf16[8,3,256,256]{3,2,1,0:T(8,128)(2,1)} %last_ref.3) | copy-start | bytes 9437188
  3.6 15.0 %copy-start.4 = (bf16[8,32,256]{2,1,0:T(8,128)(2,1)S(1)}, bf16[8,32,256]{2,1,0:T(8,128)(2,1)}, u32[]{:S(2)}) copy-start(bf16[8,32,256]{2,1,0:T(8,128)(2,1)} %v_ref.1) | copy-start | bytes 393220
  3.6 9.5 %collective-permute-start = (bf16[9,32,128]{2,1,0:T(8,128)(2,1)}, bf16[9,32,128]{2,1,0:T(8,128)(2,1)S(1)}, u32[]{:S(2)}, u32[]{:S(2)}) collective-permute-start(bf16[9,32,128]{2,1,0:T(8,128)(2,1)} %get-tuple-element.112.__.refs_0_), channel_id=1, source_target_pairs={{0,16},{1,17},{2,18},{3,19},{4,20},{5,21},{6,22},{7,23},{8,24},{9,... | collective-permute-start | bytes 221192 | tf_op jit(solution)/shard_map/ppermute | solution.py:265
  13.0 21.9 %copy-start.1 = (bf16[128,96,96]{2,1,0:T(8,128)(2,1)S(1)}, bf16[128,96,96]{2,1,0:T(8,128)(2,1)}, u32[]{:S(2)}) copy-start(bf16[128,96,96]{2,1,0:T(8,128)(2,1)} %copy.10._.coupling_ref) | copy-start | bytes 7077892
  13.9 19.7 %copy-start.8 = (s32[128]{0:T(128)S(1)}, s32[128]{0:T(128)}, u32[]{:S(2)}) copy-start(s32[128]{0:T(128)} %param.14) | copy-start | bytes 1540
  13.9 19.7 %copy-start.9 = (s32[128]{0:T(128)S(1)}, s32[128]{0:T(128)}, u32[]{:S(2)}) copy-start(s32[128]{0:T(128)} %param.15) | copy-start | bytes 1540
  13.9 6.6 %collective-permute-start.3 = (bf16[2,9,32,128]{3,2,1,0:T(8,128)(2,1)S(1)}, bf16[2,9,32,128]{3,2,1,0:T(8,128)(2,1)S(1)}, u32[]{:S(2)}, u32[]{:S(2)}) collective-permute-start(bf16[2,9,32,128]{3,2,1,0:T(8,128)(2,1)S(1)} %shard_map.97.refs_0_), channel_id=1, source_target_pairs={{0,8},{1,3},{2,10},{3,1},{4,12},{5,7},{6,14},{7,5},{8,0},{9,11},{1... | collective-permute-start | bytes 442376 | tf_op jit(solution)/shard_map/ppermute | solution.py:269
  15.5 6.2 %collective-permute-start.2 = (bf16[2,9,32,128]{3,2,1,0:T(8,128)(2,1)S(1)}, bf16[2,9,32,128]{3,2,1,0:T(8,128)(2,1)S(1)}, u32[]{:S(2)}, u32[]{:S(2)}) collective-permute-start(bf16[2,9,32,128]{3,2,1,0:T(8,128)(2,1)S(1)} %shard_map.97.refs_0_), channel_id=1, source_target_pairs={{0,4},{1,9},{2,6},{3,11},{4,0},{5,13},{6,2},{7,15},{8,12},{9,1},{1... | collective-permute-start | bytes 442376 | tf_op jit(solution)/shard_map/ppermute | solution.py:269
  17.0 5.1 %collective-permute-start.1 = (bf16[2,9,32,128]{3,2,1,0:T(8,128)(2,1)S(1)}, bf16[2,9,32,128]{3,2,1,0:T(8,128)(2,1)S(1)}, u32[]{:S(2)}, u32[]{:S(2)}) collective-permute-start(bf16[2,9,32,128]{3,2,1,0:T(8,128)(2,1)S(1)} %shard_map.97.refs_0_), channel_id=1, source_target_pairs={{0,2},{1,5},{2,0},{3,7},{4,6},{5,1},{6,4},{7,3},{8,10},{9,13},{10,... | collective-permute-start | bytes 442376 | tf_op jit(solution)/shard_map/ppermute | solution.py:269
  22.2 10.3 %collective-permute-start.8 = (bf16[4,2,9,32,128]{4,3,2,1,0:T(8,128)(2,1)S(1)}, bf16[4,2,9,32,128]{4,3,2,1,0:T(8,128)(2,1)S(1)}, u32[]{:S(2)}, u32[]{:S(2)}) collective-permute-start(bf16[4,2,9,32,128]{4,3,2,1,0:T(8,128)(2,1)S(1)} %shard_map.100.refs_0_), channel_id=1, source_target_pairs={{0,1},{1,0},{2,3},{3,2},{4,5},{5,4},{6,7},{7,6},{8,9},{9,8},{10,11... | collective-permute-start | bytes 1769480 | tf_op jit(solution)/shard_map/ppermute | solution.py:274
  22.3 5.9 %collective-permute-start.6 = (bf16[2,9,32,128]{3,2,1,0:T(8,128)(2,1)S(1)}, bf16[2,9,32,128]{3,2,1,0:T(8,128)(2,1)S(1)}, u32[]{:S(2)}, u32[]{:S(2)}) collective-permute-start(bf16[2,9,32,128]{3,2,1,0:T(8,128)(2,1)S(1)} %collective-permute-done.2.refs_2_), channel_id=1, source_target_pairs={{0,8},{1,3},{2,10},{3,1},{4,12},{5,7},{6,14},{7,5},{8,0},{9,11},{1... | collective-permute-start | bytes 442376 | tf_op jit(solution)/shard_map/ppermute | solution.py:269
  22.8 5.7 %collective-permute-start.7 = (bf16[2,9,32,128]{3,2,1,0:T(8,128)(2,1)S(1)}, bf16[2,9,32,128]{3,2,1,0:T(8,128)(2,1)S(1)}, u32[]{:S(2)}, u32[]{:S(2)}) collective-permute-start(bf16[2,9,32,128]{3,2,1,0:T(8,128)(2,1)S(1)} %collective-permute-done.3.refs_3_), channel_id=1, source_target_pairs={{0,2},{1,5},{2,0},{3,7},{4,6},{5,1},{6,4},{7,3},{8,10},{9,13},{10,... | collective-permute-start | bytes 442376 | tf_op jit(solution)/shard_map/ppermute | solution.py:269
  24.3 5.9 %collective-permute-start.5 = (bf16[2,9,32,128]{3,2,1,0:T(8,128)(2,1)S(1)}, bf16[2,9,32,128]{3,2,1,0:T(8,128)(2,1)S(1)}, u32[]{:S(2)}, u32[]{:S(2)}) collective-permute-start(bf16[2,9,32,128]{3,2,1,0:T(8,128)(2,1)S(1)} %collective-permute-done.1.refs_1_), channel_id=1, source_target_pairs={{0,4},{1,9},{2,6},{3,11},{4,0},{5,13},{6,2},{7,15},{8,12},{9,1},{1... | collective-permute-start | bytes 442376 | tf_op jit(solution)/shard_map/ppermute | solution.py:269
  24.8 7.7 %collective-permute-start.4 = (bf16[2,9,32,128]{3,2,1,0:T(8,128)(2,1)S(1)}, bf16[2,9,32,128]{3,2,1,0:T(8,128)(2,1)S(1)}, u32[]{:S(2)}, u32[]{:S(2)}) collective-permute-start(bf16[2,9,32,128]{3,2,1,0:T(8,128)(2,1)S(1)} %collective-permute-done.1.refs_1_), channel_id=1, source_target_pairs={{0,12},{1,11},{2,14},{3,9},{4,8},{5,15},{6,10},{7,13},{8,4},{9,3},... | collective-permute-start | bytes 442376 | tf_op jit(solution)/shard_map/ppermute | solution.py:269
  32.5 1.5 %collective-permute-start.9 = (bf16[2,9,32,128]{3,2,1,0:T(8,128)(2,1)S(1)}, bf16[2,9,32,128]{3,2,1,0:T(8,128)(2,1)S(1)}, u32[]{:S(2)}, u32[]{:S(2)}) collective-permute-start(bf16[2,9,32,128]{3,2,1,0:T(8,128)(2,1)S(1)} %collective-permute-done.4.refs_1_), channel_id=1, source_target_pairs={{0,1},{1,0},{2,3},{3,2},{4,5},{5,4},{6,7},{7,6},{8,9},{9,8},{10,11... | collective-permute-start | bytes 442376 | tf_op jit(solution)/shard_map/ppermute | solution.py:274
  33.0 1.4 %collective-permute-start.10 = (bf16[2,9,32,128]{3,2,1,0:T(8,128)(2,1)S(1)}, bf16[2,9,32,128]{3,2,1,0:T(8,128)(2,1)S(1)}, u32[]{:S(2)}, u32[]{:S(2)}) collective-permute-start(bf16[2,9,32,128]{3,2,1,0:T(8,128)(2,1)S(1)} %collective-permute-done.5.refs_2_), channel_id=1, source_target_pairs={{0,1},{1,0},{2,3},{3,2},{4,5},{5,4},{6,7},{7,6},{8,9},{9,8},{10,11... | collective-permute-start | bytes 442376 | tf_op jit(solution)/shard_map/ppermute | solution.py:274
  33.0 1.6 %collective-permute-start.11 = (bf16[2,9,32,128]{3,2,1,0:T(8,128)(2,1)S(1)}, bf16[2,9,32,128]{3,2,1,0:T(8,128)(2,1)S(1)}, u32[]{:S(2)}, u32[]{:S(2)}) collective-permute-start(bf16[2,9,32,128]{3,2,1,0:T(8,128)(2,1)S(1)} %collective-permute-done.6.refs_3_), channel_id=1, source_target_pairs={{0,1},{1,0},{2,3},{3,2},{4,5},{5,4},{6,7},{7,6},{8,9},{9,8},{10,11... | collective-permute-start | bytes 442376 | tf_op jit(solution)/shard_map/ppermute | solution.py:274
  33.5 1.4 %collective-permute-start.12 = (bf16[2,9,32,128]{3,2,1,0:T(8,128)(2,1)S(1)}, bf16[2,9,32,128]{3,2,1,0:T(8,128)(2,1)S(1)}, u32[]{:S(2)}, u32[]{:S(2)}) collective-permute-start(bf16[2,9,32,128]{3,2,1,0:T(8,128)(2,1)S(1)} %collective-permute-done.7.refs_4_), channel_id=1, source_target_pairs={{0,1},{1,0},{2,3},{3,2},{4,5},{5,4},{6,7},{7,6},{8,9},{9,8},{10,11... | collective-permute-start | bytes 442376 | tf_op jit(solution)/shard_map/ppermute | solution.py:274
  34.9 19.3 %copy-start.11 = (bf16[1,32,256]{2,1,0:T(8,128)(2,1)S(1)}, bf16[1,32,256]{2,1,0:T(8,128)(2,1)}, u32[]{:S(2)}) copy-start(bf16[1,32,256]{2,1,0:T(8,128)(2,1)} %get-tuple-element.153) | copy-start | bytes 49156
  38.1 23.0 %copy-start.10 = (bf16[1,32,256]{2,1,0:T(8,128)(2,1)S(1)}, bf16[1,32,256]{2,1,0:T(8,128)(2,1)}, u32[]{:S(2)}) copy-start(bf16[1,32,256]{2,1,0:T(8,128)(2,1)} %get-tuple-element.160) | copy-start | bytes 49156
  38.1 2.1 %collective-permute-start.13 = (bf16[4,2,9,32,128]{4,3,2,1,0:T(8,128)(2,1)S(1)}, bf16[4,2,9,32,128]{4,3,2,1,0:T(8,128)(2,1)S(1)}, u32[]{:S(2)}, u32[]{:S(2)}) collective-permute-start(bf16[4,2,9,32,128]{4,3,2,1,0:T(8,128)(2,1)S(1)} %get-tuple-element.127), channel_id=1, source_target_pairs={{0,1},{1,0},{2,3},{3,2},{4,5},{5,4},{6,7},{7,6},{8,9},{9,8},{10,11... | collective-permute-start | bytes 1769480 | tf_op jit(solution)/shard_map/ppermute | solution.py:274
  40.3 9.1 %collective-permute-start.17 = (bf16[4,2,9,32,128]{4,3,2,1,0:T(8,128)(2,1)S(1)}, bf16[4,2,9,32,128]{4,3,2,1,0:T(8,128)(2,1)S(1)}, u32[]{:S(2)}, u32[]{:S(2)}) collective-permute-start(bf16[4,2,9,32,128]{4,3,2,1,0:T(8,128)(2,1)S(1)} %get-tuple-element.136), channel_id=1, source_target_pairs={{0,1},{1,0},{2,3},{3,2},{4,5},{5,4},{6,7},{7,6},{8,9},{9,8},{10,11... | collective-permute-start | bytes 1769480 | tf_op jit(solution)/shard_map/ppermute | solution.py:274
  40.6 6.6 %collective-permute-start.14 = (bf16[2,9,32,128]{3,2,1,0:T(8,128)(2,1)S(1)}, bf16[2,9,32,128]{3,2,1,0:T(8,128)(2,1)S(1)}, u32[]{:S(2)}, u32[]{:S(2)}) collective-permute-start(bf16[2,9,32,128]{3,2,1,0:T(8,128)(2,1)S(1)} %get-tuple-element.133), channel_id=1, source_target_pairs={{0,4},{1,9},{2,6},{3,11},{4,0},{5,13},{6,2},{7,15},{8,12},{9,1},{1... | collective-permute-start | bytes 442376 | tf_op jit(solution)/shard_map/ppermute | solution.py:269
  41.6 5.9 %collective-permute-start.15 = (bf16[2,9,32,128]{3,2,1,0:T(8,128)(2,1)S(1)}, bf16[2,9,32,128]{3,2,1,0:T(8,128)(2,1)S(1)}, u32[]{:S(2)}, u32[]{:S(2)}) collective-permute-start(bf16[2,9,32,128]{3,2,1,0:T(8,128)(2,1)S(1)} %get-tuple-element.134), channel_id=1, source_target_pairs={{0,8},{1,3},{2,10},{3,1},{4,12},{5,7},{6,14},{7,5},{8,0},{9,11},{1... | collective-permute-start | bytes 442376 | tf_op jit(solution)/shard_map/ppermute | solution.py:269
  42.1 7.3 %collective-permute-start.16 = (bf16[2,9,32,128]{3,2,1,0:T(8,128)(2,1)S(1)}, bf16[2,9,32,128]{3,2,1,0:T(8,128)(2,1)S(1)}, u32[]{:S(2)}, u32[]{:S(2)}) collective-permute-start(bf16[2,9,32,128]{3,2,1,0:T(8,128)(2,1)S(1)} %get-tuple-element.135), channel_id=1, source_target_pairs={{0,2},{1,5},{2,0},{3,7},{4,6},{5,1},{6,4},{7,3},{8,10},{9,13},{10,... | collective-permute-start | bytes 442376 | tf_op jit(solution)/shard_map/ppermute | solution.py:269
  43.6 11.9 %collective-permute-start.21 = (bf16[2,9,32,128]{3,2,1,0:T(8,128)(2,1)S(1)}, bf16[2,9,32,128]{3,2,1,0:T(8,128)(2,1)S(1)}, u32[]{:S(2)}, u32[]{:S(2)}) collective-permute-start(bf16[2,9,32,128]{3,2,1,0:T(8,128)(2,1)S(1)} %get-tuple-element.151), channel_id=1, source_target_pairs={{0,14},{1,15},{2,12},{3,13},{4,10},{5,11},{6,8},{7,9},{8,6},{9,7},... | collective-permute-start | bytes 442376 | tf_op jit(solution)/shard_map/ppermute | solution.py:269
  49.6 10.2 %collective-permute-start.18 = (bf16[2,9,32,128]{3,2,1,0:T(8,128)(2,1)S(1)}, bf16[2,9,32,128]{3,2,1,0:T(8,128)(2,1)S(1)}, u32[]{:S(2)}, u32[]{:S(2)}) collective-permute-start(bf16[2,9,32,128]{3,2,1,0:T(8,128)(2,1)S(1)} %get-tuple-element.148), channel_id=1, source_target_pairs={{0,2},{1,5},{2,0},{3,7},{4,6},{5,1},{6,4},{7,3},{8,10},{9,13},{10,... | collective-permute-start | bytes 442376 | tf_op jit(solution)/shard_map/ppermute | solution.py:269
  52.1 7.7 %collective-permute-start.19 = (bf16[2,9,32,128]{3,2,1,0:T(8,128)(2,1)S(1)}, bf16[2,9,32,128]{3,2,1,0:T(8,128)(2,1)S(1)}, u32[]{:S(2)}, u32[]{:S(2)}) collective-permute-start(bf16[2,9,32,128]{3,2,1,0:T(8,128)(2,1)S(1)} %get-tuple-element.149), channel_id=1, source_target_pairs={{0,4},{1,9},{2,6},{3,11},{4,0},{5,13},{6,2},{7,15},{8,12},{9,1},{1... | collective-permute-start | bytes 442376 | tf_op jit(solution)/shard_map/ppermute | solution.py:269
  52.1 7.7 %collective-permute-start.20 = (bf16[2,9,32,128]{3,2,1,0:T(8,128)(2,1)S(1)}, bf16[2,9,32,128]{3,2,1,0:T(8,128)(2,1)S(1)}, u32[]{:S(2)}, u32[]{:S(2)}) collective-permute-start(bf16[2,9,32,128]{3,2,1,0:T(8,128)(2,1)S(1)} %get-tuple-element.150), channel_id=1, source_target_pairs={{0,8},{1,3},{2,10},{3,1},{4,12},{5,7},{6,14},{7,5},{8,0},{9,11},{1... | collective-permute-start | bytes 442376 | tf_op jit(solution)/shard_map/ppermute | solution.py:269
  54.2 5.6 %collective-permute-start.22 = (bf16[1,32,256]{2,1,0:T(8,128)(2,1)S(1)}, bf16[1,32,256]{2,1,0:T(8,128)(2,1)S(1)}, u32[]{:S(2)}, u32[]{:S(2)}) collective-permute-start(bf16[1,32,256]{2,1,0:T(8,128)(2,1)S(1)} %copy-done.11), channel_id=1, source_target_pairs={{1,3},{3,5},{5,7},{7,9},{9,11},{11,13},{13,15},{15,17},{17,19},{19... | collective-permute-start | bytes 49160 | tf_op jit(solution)/shard_map/ppermute | solution.py:432
  59.9 6.1 %copy-start.2 = (bf16[8,96,256]{2,1,0:T(8,128)(2,1)S(1)}, bf16[8,96,256]{2,1,0:T(8,128)(2,1)}, u32[]{:S(2)}) copy-start(bf16[8,96,256]{2,1,0:T(8,128)(2,1)} %basis_ref.3) | copy-start | bytes 1179652
  59.9 6.1 %collective-permute-start.23 = (bf16[9,32,128]{2,1,0:T(8,128)(2,1)S(1)}, bf16[9,32,128]{2,1,0:T(8,128)(2,1)S(1)}, u32[]{:S(2)}, u32[]{:S(2)}) collective-permute-start(bf16[9,32,128]{2,1,0:T(8,128)(2,1)S(1)} %get-tuple-element.159), channel_id=1, source_target_pairs={{0,16},{1,17},{2,18},{3,19},{4,20},{5,21},{6,22},{7,23},{8,24},{9,... | collective-permute-start | bytes 221192 | tf_op jit(solution)/shard_map/ppermute | solution.py:265
  61.1 1.2 collective-permute-start.24
  61.1 1.3 %collective-permute-start.25 = (bf16[1,32,256]{2,1,0:T(8,128)(2,1)S(1)}, bf16[1,32,256]{2,1,0:T(8,128)(2,1)S(1)}, u32[]{:S(2)}, u32[]{:S(2)}) collective-permute-start(bf16[1,32,256]{2,1,0:T(8,128)(2,1)S(1)} %collective-permute-done.22), channel_id=1, source_target_pairs={{0,1},{1,0},{2,3},{3,2},{4,5},{5,4},{6,7},{7,6},{8,9},{9,8},{10,11... | collective-permute-start | bytes 49160 | tf_op jit(solution)/shard_map/ppermute | solution.py:274
  67.7 5.5 %collective-permute-start.26 = (bf16[9,32,128]{2,1,0:T(8,128)(2,1)S(1)}, bf16[9,32,128]{2,1,0:T(8,128)(2,1)S(1)}, u32[]{:S(2)}, u32[]{:S(2)}) collective-permute-start(bf16[9,32,128]{2,1,0:T(8,128)(2,1)S(1)} %get-tuple-element.166.refs_0_), channel_id=1, source_target_pairs={{0,16},{1,17},{2,18},{3,19},{4,20},{5,21},{6,22},{7,23},{8,24},{9,... | collective-permute-start | bytes 221192 | tf_op jit(solution)/shard_map/ppermute | solution.py:265
  73.2 6.5 %collective-permute-start.29 = (bf16[2,9,32,128]{3,2,1,0:T(8,128)(2,1)S(1)}, bf16[2,9,32,128]{3,2,1,0:T(8,128)(2,1)S(1)}, u32[]{:S(2)}, u32[]{:S(2)}) collective-permute-start(bf16[2,9,32,128]{3,2,1,0:T(8,128)(2,1)S(1)} %shard_map.107.refs_0_), channel_id=1, source_target_pairs={{0,8},{1,3},{2,10},{3,1},{4,12},{5,7},{6,14},{7,5},{8,0},{9,11},{1... | collective-permute-start | bytes 442376 | tf_op jit(solution)/shard_map/ppermute | solution.py:269
  73.3 6.8 %collective-permute-start.28 = (bf16[2,9,32,128]{3,2,1,0:T(8,128)(2,1)S(1)}, bf16[2,9,32,128]{3,2,1,0:T(8,128)(2,1)S(1)}, u32[]{:S(2)}, u32[]{:S(2)}) collective-permute-start(bf16[2,9,32,128]{3,2,1,0:T(8,128)(2,1)S(1)} %shard_map.107.refs_0_), channel_id=1, source_target_pairs={{0,4},{1,9},{2,6},{3,11},{4,0},{5,13},{6,2},{7,15},{8,12},{9,1},{1... | collective-permute-start | bytes 442376 | tf_op jit(solution)/shard_map/ppermute | solution.py:269
  74.6 5.4 %collective-permute-start.27 = (bf16[2,9,32,128]{3,2,1,0:T(8,128)(2,1)S(1)}, bf16[2,9,32,128]{3,2,1,0:T(8,128)(2,1)S(1)}, u32[]{:S(2)}, u32[]{:S(2)}) collective-permute-start(bf16[2,9,32,128]{3,2,1,0:T(8,128)(2,1)S(1)} %shard_map.107.refs_0_), channel_id=1, source_target_pairs={{0,2},{1,5},{2,0},{3,7},{4,6},{5,1},{6,4},{7,3},{8,10},{9,13},{10,... | collective-permute-start | bytes 442376 | tf_op jit(solution)/shard_map/ppermute | solution.py:269
  77.1 10.5 %collective-permute-start.33 = (bf16[2,9,32,128]{3,2,1,0:T(8,128)(2,1)S(1)}, bf16[2,9,32,128]{3,2,1,0:T(8,128)(2,1)S(1)}, u32[]{:S(2)}, u32[]{:S(2)}) collective-permute-start(bf16[2,9,32,128]{3,2,1,0:T(8,128)(2,1)S(1)} %shard_map.107.refs_0_), channel_id=1, source_target_pairs={{0,14},{1,15},{2,12},{3,13},{4,10},{5,11},{6,8},{7,9},{8,6},{9,7},... | collective-permute-start | bytes 442376 | tf_op jit(solution)/shard_map/ppermute | solution.py:269
  80.0 8.1 %collective-permute-start.30 = (bf16[2,9,32,128]{3,2,1,0:T(8,128)(2,1)S(1)}, bf16[2,9,32,128]{3,2,1,0:T(8,128)(2,1)S(1)}, u32[]{:S(2)}, u32[]{:S(2)}) collective-permute-start(bf16[2,9,32,128]{3,2,1,0:T(8,128)(2,1)S(1)} %collective-permute-done.27.refs_1_), channel_id=1, source_target_pairs={{0,4},{1,9},{2,6},{3,11},{4,0},{5,13},{6,2},{7,15},{8,12},{9,1},{1... | collective-permute-start | bytes 442376 | tf_op jit(solution)/shard_map/ppermute | solution.py:269
  81.1 6.5 %collective-permute-start.34 = (bf16[1,32,256]{2,1,0:T(8,128)(2,1)S(1)}, bf16[1,32,256]{2,1,0:T(8,128)(2,1)S(1)}, u32[]{:S(2)}, u32[]{:S(2)}) collective-permute-start(bf16[1,32,256]{2,1,0:T(8,128)(2,1)S(1)} %get-tuple-element.173), channel_id=1, source_target_pairs={{1,3},{3,5},{5,7},{7,9},{9,11},{11,13},{13,15},{15,17},{17,19},{19... | collective-permute-start | bytes 49160 | tf_op jit(solution)/shard_map/ppermute | solution.py:416
  82.6 7.5 %collective-permute-start.32 = (bf16[2,9,32,128]{3,2,1,0:T(8,128)(2,1)S(1)}, bf16[2,9,32,128]{3,2,1,0:T(8,128)(2,1)S(1)}, u32[]{:S(2)}, u32[]{:S(2)}) collective-permute-start(bf16[2,9,32,128]{3,2,1,0:T(8,128)(2,1)S(1)} %collective-permute-done.28.refs_2_), channel_id=1, source_target_pairs={{0,8},{1,3},{2,10},{3,1},{4,12},{5,7},{6,14},{7,5},{8,0},{9,11},{1... | collective-permute-start | bytes 442376 | tf_op jit(solution)/shard_map/ppermute | solution.py:269
  86.9 5.1 %collective-permute-start.31 = (bf16[2,9,32,128]{3,2,1,0:T(8,128)(2,1)S(1)}, bf16[2,9,32,128]{3,2,1,0:T(8,128)(2,1)S(1)}, u32[]{:S(2)}, u32[]{:S(2)}) collective-permute-start(bf16[2,9,32,128]{3,2,1,0:T(8,128)(2,1)S(1)} %collective-permute-done.29.refs_4_), channel_id=1, source_target_pairs={{0,2},{1,5},{2,0},{3,7},{4,6},{5,1},{6,4},{7,3},{8,10},{9,13},{10,... | collective-permute-start | bytes 442376 | tf_op jit(solution)/shard_map/ppermute | solution.py:269
  87.6 4.5 %collective-permute-start.35 = (bf16[2,9,32,128]{3,2,1,0:T(8,128)(2,1)S(1)}, bf16[2,9,32,128]{3,2,1,0:T(8,128)(2,1)S(1)}, u32[]{:S(2)}, u32[]{:S(2)}) collective-permute-start(bf16[2,9,32,128]{3,2,1,0:T(8,128)(2,1)S(1)} %shard_map.107.refs_0_), channel_id=1, source_target_pairs={{0,1},{1,0},{2,3},{3,2},{4,5},{5,4},{6,7},{7,6},{8,9},{9,8},{10,11... | collective-permute-start | bytes 442376 | tf_op jit(solution)/shard_map/ppermute | solution.py:274
  87.6 5.0 %collective-permute-start.36 = (bf16[2,9,32,128]{3,2,1,0:T(8,128)(2,1)S(1)}, bf16[2,9,32,128]{3,2,1,0:T(8,128)(2,1)S(1)}, u32[]{:S(2)}, u32[]{:S(2)}) collective-permute-start(bf16[2,9,32,128]{3,2,1,0:T(8,128)(2,1)S(1)} %collective-permute-done.27.refs_1_), channel_id=1, source_target_pairs={{0,1},{1,0},{2,3},{3,2},{4,5},{5,4},{6,7},{7,6},{8,9},{9,8},{10,11... | collective-permute-start | bytes 442376 | tf_op jit(solution)/shard_map/ppermute | solution.py:274
  88.1 4.5 %collective-permute-start.37 = (bf16[2,9,32,128]{3,2,1,0:T(8,128)(2,1)S(1)}, bf16[2,9,32,128]{3,2,1,0:T(8,128)(2,1)S(1)}, u32[]{:S(2)}, u32[]{:S(2)}) collective-permute-start(bf16[2,9,32,128]{3,2,1,0:T(8,128)(2,1)S(1)} %collective-permute-done.28.refs_2_), channel_id=1, source_target_pairs={{0,1},{1,0},{2,3},{3,2},{4,5},{5,4},{6,7},{7,6},{8,9},{9,8},{10,11... | collective-permute-start | bytes 442376 | tf_op jit(solution)/shard_map/ppermute | solution.py:274
  90.1 3.1 %collective-permute-start.39 = (bf16[2,9,32,128]{3,2,1,0:T(8,128)(2,1)S(1)}, bf16[2,9,32,128]{3,2,1,0:T(8,128)(2,1)S(1)}, u32[]{:S(2)}, u32[]{:S(2)}) collective-permute-start(bf16[2,9,32,128]{3,2,1,0:T(8,128)(2,1)S(1)} %collective-permute-done.29.refs_4_), channel_id=1, source_target_pairs={{0,1},{1,0},{2,3},{3,2},{4,5},{5,4},{6,7},{7,6},{8,9},{9,8},{10,11... | collective-permute-start | bytes 442376 | tf_op jit(solution)/shard_map/ppermute | solution.py:274
  92.1 1.4 %collective-permute-start.38 = (bf16[2,9,32,128]{3,2,1,0:T(8,128)(2,1)S(1)}, bf16[2,9,32,128]{3,2,1,0:T(8,128)(2,1)S(1)}, u32[]{:S(2)}, u32[]{:S(2)}) collective-permute-start(bf16[2,9,32,128]{3,2,1,0:T(8,128)(2,1)S(1)} %collective-permute-done.30.refs_3_), channel_id=1, source_target_pairs={{0,1},{1,0},{2,3},{3,2},{4,5},{5,4},{6,7},{7,6},{8,9},{9,8},{10,11... | collective-permute-start | bytes 442376 | tf_op jit(solution)/shard_map/ppermute | solution.py:274
  92.1 1.6 %collective-permute-start.40 = (bf16[2,9,32,128]{3,2,1,0:T(8,128)(2,1)S(1)}, bf16[2,9,32,128]{3,2,1,0:T(8,128)(2,1)S(1)}, u32[]{:S(2)}, u32[]{:S(2)}) collective-permute-start(bf16[2,9,32,128]{3,2,1,0:T(8,128)(2,1)S(1)} %collective-permute-done.31.refs_5_), channel_id=1, source_target_pairs={{0,1},{1,0},{2,3},{3,2},{4,5},{5,4},{6,7},{7,6},{8,9},{9,8},{10,11... | collective-permute-start | bytes 442376 | tf_op jit(solution)/shard_map/ppermute | solution.py:274
  92.6 1.4 %collective-permute-start.41 = (bf16[2,9,32,128]{3,2,1,0:T(8,128)(2,1)S(1)}, bf16[2,9,32,128]{3,2,1,0:T(8,128)(2,1)S(1)}, u32[]{:S(2)}, u32[]{:S(2)}) collective-permute-start(bf16[2,9,32,128]{3,2,1,0:T(8,128)(2,1)S(1)} %collective-permute-done.32.refs_6_), channel_id=1, source_target_pairs={{0,1},{1,0},{2,3},{3,2},{4,5},{5,4},{6,7},{7,6},{8,9},{9,8},{10,11... | collective-permute-start | bytes 442376 | tf_op jit(solution)/shard_map/ppermute | solution.py:274
  92.7 1.5 %collective-permute-start.42 = (bf16[2,9,32,128]{3,2,1,0:T(8,128)(2,1)S(1)}, bf16[2,9,32,128]{3,2,1,0:T(8,128)(2,1)S(1)}, u32[]{:S(2)}, u32[]{:S(2)}) collective-permute-start(bf16[2,9,32,128]{3,2,1,0:T(8,128)(2,1)S(1)} %collective-permute-done.33.refs_7_), channel_id=1, source_target_pairs={{0,1},{1,0},{2,3},{3,2},{4,5},{5,4},{6,7},{7,6},{8,9},{9,8},{10,11... | collective-permute-start | bytes 442376 | tf_op jit(solution)/shard_map/ppermute | solution.py:274
  97.4 2.1 %collective-permute-start.43 = (bf16[4,2,9,32,128]{4,3,2,1,0:T(8,128)(2,1)S(1)}, bf16[4,2,9,32,128]{4,3,2,1,0:T(8,128)(2,1)S(1)}, u32[]{:S(2)}, u32[]{:S(2)}) collective-permute-start(bf16[4,2,9,32,128]{4,3,2,1,0:T(8,128)(2,1)S(1)} %get-tuple-element.184), channel_id=1, source_target_pairs={{0,1},{1,0},{2,3},{3,2},{4,5},{5,4},{6,7},{7,6},{8,9},{9,8},{10,11... | collective-permute-start | bytes 1769480 | tf_op jit(solution)/shard_map/ppermute | solution.py:274
  99.6 10.1 %collective-permute-start.48 = (bf16[4,2,9,32,128]{4,3,2,1,0:T(8,128)(2,1)S(1)}, bf16[4,2,9,32,128]{4,3,2,1,0:T(8,128)(2,1)S(1)}, u32[]{:S(2)}, u32[]{:S(2)}) collective-permute-start(bf16[4,2,9,32,128]{4,3,2,1,0:T(8,128)(2,1)S(1)} %get-tuple-element.194), channel_id=1, source_target_pairs={{0,1},{1,0},{2,3},{3,2},{4,5},{5,4},{6,7},{7,6},{8,9},{9,8},{10,11... | collective-permute-start | bytes 1769480 | tf_op jit(solution)/shard_map/ppermute | solution.py:274
  100.0 6.4 %collective-permute-start.44 = (bf16[2,9,32,128]{3,2,1,0:T(8,128)(2,1)S(1)}, bf16[2,9,32,128]{3,2,1,0:T(8,128)(2,1)S(1)}, u32[]{:S(2)}, u32[]{:S(2)}) collective-permute-start(bf16[2,9,32,128]{3,2,1,0:T(8,128)(2,1)S(1)} %get-tuple-element.190), channel_id=1, source_target_pairs={{0,4},{1,9},{2,6},{3,11},{4,0},{5,13},{6,2},{7,15},{8,12},{9,1},{1... | collective-permute-start | bytes 442376 | tf_op jit(solution)/shard_map/ppermute | solution.py:269
  101.2 6.3 %collective-permute-start.45 = (bf16[2,9,32,128]{3,2,1,0:T(8,128)(2,1)S(1)}, bf16[2,9,32,128]{3,2,1,0:T(8,128)(2,1)S(1)}, u32[]{:S(2)}, u32[]{:S(2)}) collective-permute-start(bf16[2,9,32,128]{3,2,1,0:T(8,128)(2,1)S(1)} %get-tuple-element.191), channel_id=1, source_target_pairs={{0,8},{1,3},{2,10},{3,1},{4,12},{5,7},{6,14},{7,5},{8,0},{9,11},{1... | collective-permute-start | bytes 442376 | tf_op jit(solution)/shard_map/ppermute | solution.py:269
  101.8 6.7 %collective-permute-start.46 = (bf16[2,9,32,128]{3,2,1,0:T(8,128)(2,1)S(1)}, bf16[2,9,32,128]{3,2,1,0:T(8,128)(2,1)S(1)}, u32[]{:S(2)}, u32[]{:S(2)}) collective-permute-start(bf16[2,9,32,128]{3,2,1,0:T(8,128)(2,1)S(1)} %get-tuple-element.192), channel_id=1, source_target_pairs={{0,2},{1,5},{2,0},{3,7},{4,6},{5,1},{6,4},{7,3},{8,10},{9,13},{10,... | collective-permute-start | bytes 442376 | tf_op jit(solution)/shard_map/ppermute | solution.py:269
  102.3 7.5 %collective-permute-start.47 = (bf16[2,9,32,128]{3,2,1,0:T(8,128)(2,1)S(1)}, bf16[2,9,32,128]{3,2,1,0:T(8,128)(2,1)S(1)}, u32[]{:S(2)}, u32[]{:S(2)}) collective-permute-start(bf16[2,9,32,128]{3,2,1,0:T(8,128)(2,1)S(1)} %get-tuple-element.193), channel_id=1, source_target_pairs={{0,12},{1,11},{2,14},{3,9},{4,8},{5,15},{6,10},{7,13},{8,4},{9,3},... | collective-permute-start | bytes 442376 | tf_op jit(solution)/shard_map/ppermute | solution.py:269
  110.0 5.5 %collective-permute-start.49 = (bf16[2,9,32,128]{3,2,1,0:T(8,128)(2,1)S(1)}, bf16[2,9,32,128]{3,2,1,0:T(8,128)(2,1)S(1)}, u32[]{:S(2)}, u32[]{:S(2)}) collective-permute-start(bf16[2,9,32,128]{3,2,1,0:T(8,128)(2,1)S(1)} %get-tuple-element.207), channel_id=1, source_target_pairs={{0,2},{1,5},{2,0},{3,7},{4,6},{5,1},{6,4},{7,3},{8,10},{9,13},{10,... | collective-permute-start | bytes 442376 | tf_op jit(solution)/shard_map/ppermute | solution.py:269
  110.7 5.1 %collective-permute-start.50 = (bf16[2,9,32,128]{3,2,1,0:T(8,128)(2,1)S(1)}, bf16[2,9,32,128]{3,2,1,0:T(8,128)(2,1)S(1)}, u32[]{:S(2)}, u32[]{:S(2)}) collective-permute-start(bf16[2,9,32,128]{3,2,1,0:T(8,128)(2,1)S(1)} %get-tuple-element.208), channel_id=1, source_target_pairs={{0,4},{1,9},{2,6},{3,11},{4,0},{5,13},{6,2},{7,15},{8,12},{9,1},{1... | collective-permute-start | bytes 442376 | tf_op jit(solution)/shard_map/ppermute | solution.py:269
  111.5 5.1 %collective-permute-start.51 = (bf16[2,9,32,128]{3,2,1,0:T(8,128)(2,1)S(1)}, bf16[2,9,32,128]{3,2,1,0:T(8,128)(2,1)S(1)}, u32[]{:S(2)}, u32[]{:S(2)}) collective-permute-start(bf16[2,9,32,128]{3,2,1,0:T(8,128)(2,1)S(1)} %get-tuple-element.209), channel_id=1, source_target_pairs={{0,8},{1,3},{2,10},{3,1},{4,12},{5,7},{6,14},{7,5},{8,0},{9,11},{1... | collective-permute-start | bytes 442376 | tf_op jit(solution)/shard_map/ppermute | solution.py:269
  116.8 6.1 %collective-permute-start.52 = (bf16[9,32,128]{2,1,0:T(8,128)(2,1)S(1)}, bf16[9,32,128]{2,1,0:T(8,128)(2,1)S(1)}, u32[]{:S(2)}, u32[]{:S(2)}) collective-permute-start(bf16[9,32,128]{2,1,0:T(8,128)(2,1)S(1)} %get-tuple-element.216), channel_id=1, source_target_pairs={{0,16},{1,17},{2,18},{3,19},{4,20},{5,21},{6,22},{7,23},{8,24},{9,... | collective-permute-start | bytes 221192 | tf_op jit(solution)/shard_map/ppermute | solution.py:265
  119.4 1.2 collective-permute-start.53
  119.4 1.3 %collective-permute-start.54 = (bf16[1,32,256]{2,1,0:T(8,128)(2,1)S(1)}, bf16[1,32,256]{2,1,0:T(8,128)(2,1)S(1)}, u32[]{:S(2)}, u32[]{:S(2)}) collective-permute-start(bf16[1,32,256]{2,1,0:T(8,128)(2,1)S(1)} %collective-permute-done.34), channel_id=1, source_target_pairs={{0,1},{1,0},{2,3},{3,2},{4,5},{5,4},{6,7},{7,6},{8,9},{9,8},{10,11... | collective-permute-start | bytes 49160 | tf_op jit(solution)/shard_map/ppermute | solution.py:274
  (3 other events, 13.1 us)
